TPU v7x, 32 devices: a whole 2x2x4 slice. The times are simulated.
32 devices in a mesh: wide: 16 (over z, x, core), narrow: 2 (over y).
Axes of the slice: x: 2, y: 2, z: 4, core: 2. Of those that a mesh axis runs over, the one named last changes fastest.
Arguments:
- tokens: bfloat16 [4096, 1024], P('wide', 'narrow'), may hold values from -6 to 6
- norm_gain: float32 [1024], replicated, may hold values from 0.1 to 1.9
- in_weight: bfloat16 [1024, 2, 2048], P(None, None, 'narrow'), may hold values from -0.1875 to 0.1875
- conv_weight: float32 [4, 2048], P(None, 'narrow'), may hold values from -3 to 3
- conv_bias: float32 [2048], P('narrow'), may hold values from -3 to 3
- select_weight: bfloat16 [96, 2048], P(None, 'narrow'), may hold values from -0.125 to 0.125
- step_weight: bfloat16 [64, 2048], P(None, 'narrow'), may hold values from -0.75 to 0.75
- step_bias: float32 [2048], P('narrow'), may hold values from -6 to -2
- decay_log: float32 [16, 2048], P(None, 'narrow'), may hold values from -10 to 1
- skip_gain: float32 [2048], P('narrow'), may hold values from 0.5 to 1.5
- out_weight: bfloat16 [2048, 1024], P('narrow'), may hold values from -0.125 to 0.125
- segment_ids: int32 [4096], P('wide'), may hold values from 0 to 16, as said below
- cotangent: bfloat16 [4096, 1024], P('wide', 'narrow'), may hold values from -6 to 6
Outputs:
- layer_out: bfloat16 [4096, 1024], P('wide', 'narrow')
- tokens_grad: bfloat16 [4096, 1024], P('wide', 'narrow')
- norm_gain_grad: float32 [1024], replicated
- in_weight_grad: float32 [1024, 2, 2048], P(None, None, 'narrow')
- conv_weight_grad: float32 [4, 2048], P(None, 'narrow')
- conv_bias_grad: float32 [2048], P('narrow')
- select_weight_grad: float32 [96, 2048], P(None, 'narrow')
- step_weight_grad: float32 [64, 2048], P(None, 'narrow')
- step_bias_grad: float32 [2048], P('narrow')
- decay_log_grad: float32 [16, 2048], P(None, 'narrow')
- skip_gain_grad: float32 [2048], P('narrow')
- out_weight_grad: float32 [2048, 1024], P('narrow')
Inputs may be any that keep to these rules, and one draw needn't show every extreme that they name: `segment_ids`: segment ids never fall along the tokens and the first is 0; they rise by one at a time, exactly 4 times in each aligned block of 1024 tokens, and never at the first token of an aligned block of 256 tokens.
All inputs are finite; a program needn't handle non-finite values.
Results may differ from a plain program's by a relative error of at most 0.0065.
The roundings to bfloat16 on the way count: a program that leaves them out, or rounds other values in their place, can miss the bound.
Values may be sent and summed in bfloat16 or wider, within the bound.
No kernel may reach another device: no remote copies, remote signals or barrier semaphores. Data moves between devices by JAX's collectives and lax.ppermute only.
A program may use at most 128 MiB of HBM per device.

v0:
```python
import jax
import jax.numpy as jnp
from jax import lax
from jax.sharding import PartitionSpec as P

epsilon = 1e-05
block_rows = 64
unroll_rows = 8


def passed_along(array, axis, by):
    peers = lax.axis_size(axis)
    pairs = [(i, i + by) for i in range(peers) if 0 <= i + by < peers]
    return lax.ppermute(array, axis, pairs)


def carried_in(part, axis, combine, identity):
    place = lax.axis_index(axis)
    gathered = jax.tree.map(lambda a: lax.all_gather(a, axis), part)
    state = jax.tree.map(lambda a, e: jnp.zeros_like(a) + jnp.asarray(e, a.dtype), part, identity)

    def one(step, state):
        return combine(
            state, jax.tree.map(lambda a: lax.dynamic_index_in_dim(a, step, 0, False), gathered)
        )

    return lax.fori_loop(0, place, one, state)


def carried_in_2(array, axis, combine, identity):
    peers, position = (lax.axis_size(axis), lax.axis_index(axis))
    everything = jax.tree.map(
        lambda part, kind: lax.all_gather(part.astype(kind), axis),
        array,
        (jnp.bfloat16, jnp.bfloat16),
    )
    start = jax.tree.map(
        lambda part, zero: jnp.broadcast_to(jnp.asarray(zero, part.dtype), part.shape),
        array,
        identity,
    )

    def step(k, before):
        at = peers - 1 - k
        reached = at > position
        new = combine(
            before, jax.tree.map(lambda part, own: part[at].astype(own.dtype), everything, array)
        )
        return jax.tree.map(lambda a, b: jnp.where(reached, a, b), new, before)

    return lax.fori_loop(0, peers, step, start)


def silu_of(values):
    return values * jax.nn.sigmoid(values)


def silu_slope(values):
    logistic = jax.nn.sigmoid(values)
    return logistic * (1.0 + values * (1.0 - logistic))


def in_blocks(operand):
    return operand.reshape((operand.shape[0] // block_rows, block_rows) + operand.shape[1:])


def compose(earlier, later):
    return (later[0] * earlier[0], later[1] + later[0] * earlier[1])


def row_update(current, decay_mat, step_row, act_row, in_row, keep_row):
    factor = jnp.exp(step_row[None, :] * decay_mat) * keep_row
    return factor * current + in_row[:, None] * (step_row * act_row)[None, :]


def final_state(initial, decay_mat, step_size, act_float, in_coef, keep_flag):

    def final_inner_row(current, row):
        step_row, act_row, in_row, keep_row = row
        return (row_update(current, decay_mat, step_row, act_row, in_row, keep_row), None)

    def final_advance(current, pieces):
        current, ignored = lax.scan(final_inner_row, current, pieces, unroll=unroll_rows)
        return (current, None)

    result_state, ignored = lax.scan(
        final_advance,
        initial,
        (in_blocks(step_size), in_blocks(act_float), in_blocks(in_coef), in_blocks(keep_flag)),
    )
    return result_state


def read_states(initial, decay_mat, step_size, act_float, in_coef, read_coef, keep_flag):

    def read_inner_row(current, row):
        step_row, act_row, in_row, read_row, keep_row = row
        current = row_update(current, decay_mat, step_row, act_row, in_row, keep_row)
        return (current, jnp.sum(read_row[:, None] * current, axis=0))

    def read_advance(current, pieces):
        begin_state = current
        current, rows_out = lax.scan(read_inner_row, current, pieces, unroll=unroll_rows)
        return (current, (begin_state, rows_out))

    ignored, (starts, outputs) = lax.scan(
        read_advance,
        initial,
        (
            in_blocks(step_size),
            in_blocks(act_float),
            in_blocks(in_coef),
            in_blocks(read_coef),
            in_blocks(keep_flag),
        ),
    )
    return (starts, outputs.reshape(step_size.shape))


def start_adjoint(decay_mat, step_size, read_coef, keep_flag, scan_grad):

    def start_inner_row(adjoint, row):
        step_row, read_row, keep_row, grad_row = row
        summed = read_row[:, None] * grad_row[None, :] + adjoint
        return (jnp.exp(step_row[None, :] * decay_mat) * keep_row * summed, None)

    def start_retreat(adjoint, pieces):
        adjoint, ignored = lax.scan(
            start_inner_row, adjoint, pieces, reverse=True, unroll=unroll_rows
        )
        return (adjoint, None)

    initial = jnp.zeros(decay_mat.shape, jnp.float32)
    result_adjoint, ignored = lax.scan(
        start_retreat,
        initial,
        (in_blocks(step_size), in_blocks(read_coef), in_blocks(keep_flag), in_blocks(scan_grad)),
        reverse=True,
    )
    return result_adjoint


def scan_backward(
    tail_adjoint, starts, decay_mat, step_size, act_float, in_coef, read_coef, keep_flag, scan_grad
):

    def forward_row(current, row):
        step_row, act_row, in_row, keep_row = row
        after = row_update(current, decay_mat, step_row, act_row, in_row, keep_row)
        return (after, (current, after))

    def backward_row(carried, row):
        adjoint, decay_grad = carried
        step_row, act_row, in_row, read_row, keep_row, grad_row, before, after = row
        factor = jnp.exp(step_row[None, :] * decay_mat)
        summed = read_row[:, None] * grad_row[None, :] + adjoint
        read_out = jnp.sum(grad_row[None, :] * after, axis=1)
        in_out = jnp.sum(summed * (step_row * act_row)[None, :], axis=1)
        weighted = jnp.sum(summed * in_row[:, None], axis=0)
        act_out = weighted * step_row
        held = summed * keep_row * before * factor
        step_out = weighted * act_row + jnp.sum(held * decay_mat, axis=0)
        decay_grad = decay_grad + held * step_row[None, :]
        adjoint = factor * keep_row * summed
        return ((adjoint, decay_grad), (step_out, act_out, in_out, read_out))

    def scan_retreat(carried, pieces):
        begin_state, step_blk, act_blk, in_blk, read_blk, keep_blk, grad_blk = pieces
        ignored, (befores, afters) = lax.scan(
            forward_row, begin_state, (step_blk, act_blk, in_blk, keep_blk), unroll=unroll_rows
        )
        carried, rows_out = lax.scan(
            backward_row,
            carried,
            (step_blk, act_blk, in_blk, read_blk, keep_blk, grad_blk, befores, afters),
            reverse=True,
            unroll=unroll_rows,
        )
        return (carried, rows_out)

    initial = (tail_adjoint, jnp.zeros(decay_mat.shape, jnp.float32))
    (ignored, decay_grad), (step_grad, act_grad, in_grad, read_grad) = lax.scan(
        scan_retreat,
        initial,
        (
            starts,
            in_blocks(step_size),
            in_blocks(act_float),
            in_blocks(in_coef),
            in_blocks(read_coef),
            in_blocks(keep_flag),
            in_blocks(scan_grad),
        ),
        reverse=True,
    )
    row_count = step_size.shape[0]
    return (
        step_grad.reshape(step_size.shape),
        act_grad.reshape(step_size.shape),
        in_grad.reshape(row_count, -1),
        read_grad.reshape(row_count, -1),
        decay_grad,
    )


def local(
    tokens,
    norm_gain,
    in_weight,
    conv_weight,
    conv_bias,
    select_weight,
    step_weight,
    step_bias,
    decay_log,
    skip_gain,
    out_weight,
    segment_ids,
    cotangent,
):
    row_count = tokens.shape[0]
    tap_count = conv_weight.shape[0]
    lag_rows = tap_count - 1
    rank_size = step_weight.shape[0]
    state_count = decay_log.shape[0]
    contract_rows = (((0,), (0,)), ((), ()))
    contract_last = (((1,), (1,)), ((), ()))
    whole = lax.all_gather(tokens, "narrow", axis=1, tiled=True).astype(jnp.float32)
    inverse = lax.rsqrt(jnp.mean(whole * whole, axis=1, keepdims=True) + epsilon)
    normed = (whole * inverse * norm_gain).astype(jnp.bfloat16)
    projected = jnp.einsum(
        "td,dce->tce", normed, in_weight, preferred_element_type=jnp.float32
    ).astype(jnp.bfloat16)
    inner_half = projected[:, 0].astype(jnp.float32)
    gate_half = projected[:, 1].astype(jnp.float32)
    seg_float = segment_ids.astype(jnp.float32)
    prior_rows, prior_seg = passed_along(
        (inner_half[row_count - lag_rows :], seg_float[row_count - lag_rows :]), "wide", 1
    )
    extended = jnp.concatenate([prior_rows, inner_half], axis=0)
    ext_seg = jnp.concatenate([prior_seg, seg_float], axis=0)
    masks = []
    convolved = conv_bias + jnp.zeros(inner_half.shape, jnp.float32)
    for tap_index in range(tap_count):
        tap_mask = jnp.where(ext_seg[tap_index : tap_index + row_count] == seg_float, 1.0, 0.0)[
            :, None
        ]
        masks.append(tap_mask)
        convolved = (
            convolved
            + conv_weight[tap_index] * extended[tap_index : tap_index + row_count] * tap_mask
        )
    keep_flag = jnp.where(
        seg_float == jnp.concatenate([prior_seg[lag_rows - 1 :], seg_float[:-1]]), 1.0, 0.0
    )
    activated = silu_of(convolved).astype(jnp.bfloat16)
    act_float = activated.astype(jnp.float32)
    all_act, all_weight = (
        lax.all_gather(activated, "narrow", axis=1, tiled=True),
        lax.all_gather(select_weight, "narrow", axis=1, tiled=True),
    )
    selected = lax.dot_general(
        all_act, all_weight, contract_last, preferred_element_type=jnp.float32
    )
    step_low = selected[:, :rank_size].astype(jnp.bfloat16)
    in_coef = selected[:, rank_size : rank_size + state_count]
    read_coef = selected[:, rank_size + state_count :]
    step_pre = jnp.dot(step_low, step_weight, preferred_element_type=jnp.float32) + step_bias
    step_size = jax.nn.softplus(step_pre)
    decay_mat = -jnp.exp(decay_log)
    zero_state = jnp.zeros(decay_mat.shape, jnp.float32)
    local_end = final_state(zero_state, decay_mat, step_size, act_float, in_coef, keep_flag)
    device_decay = jnp.exp(decay_mat * jnp.sum(step_size, axis=0)[None, :]) * jnp.prod(keep_flag)
    identity = (jnp.ones(decay_mat.shape, jnp.float32), zero_state)
    ignored, entry_state = carried_in((device_decay, local_end), "wide", compose, identity)
    starts, scanned = read_states(
        entry_state, decay_mat, step_size, act_float, in_coef, read_coef, keep_flag
    )
    scanned = scanned + skip_gain * act_float
    gate_act = silu_of(gate_half)
    gated = (scanned * gate_act).astype(jnp.bfloat16)
    out_part = jnp.dot(gated, out_weight, preferred_element_type=jnp.float32)
    out_mine = lax.psum_scatter(out_part, "narrow", scatter_dimension=1, tiled=True)
    layer_out = (tokens.astype(jnp.float32) + out_mine).astype(jnp.bfloat16)
    cot_whole = lax.all_gather(cotangent, "narrow", axis=1, tiled=True)
    out_weight_grad = lax.dot_general(
        gated, cot_whole, contract_rows, preferred_element_type=jnp.float32
    )
    gated_grad = lax.dot_general(
        cot_whole, out_weight, contract_last, preferred_element_type=jnp.float32
    )
    scan_grad = gated_grad * gate_act
    gate_grad = (gated_grad * scanned * silu_slope(gate_half)).astype(jnp.bfloat16)
    skip_gain_grad = jnp.sum(scan_grad * act_float, axis=0)
    local_adjoint = start_adjoint(decay_mat, step_size, read_coef, keep_flag, scan_grad)
    ignored_total, tail_adjoint = carried_in_2(
        (device_decay, local_adjoint), "wide", compose, identity
    )
    step_grad, act_grad, in_grad, read_grad, decay_grad = scan_backward(
        tail_adjoint,
        starts,
        decay_mat,
        step_size,
        act_float,
        in_coef,
        read_coef,
        keep_flag,
        scan_grad,
    )
    act_grad = act_grad + skip_gain * scan_grad
    pre_grad = (step_grad * jax.nn.sigmoid(step_pre)).astype(jnp.bfloat16)
    step_bias_grad = jnp.sum(pre_grad.astype(jnp.float32), axis=0)
    step_weight_grad = lax.dot_general(
        step_low, pre_grad, contract_rows, preferred_element_type=jnp.float32
    )
    low_grad = lax.dot_general(
        pre_grad, step_weight, contract_last, preferred_element_type=jnp.float32
    )
    select_grad = lax.psum(
        jnp.concatenate([low_grad, in_grad, read_grad], axis=1), "narrow"
    ).astype(jnp.bfloat16)
    act_total = act_grad + jnp.dot(select_grad, select_weight, preferred_element_type=jnp.float32)
    select_weight_grad = lax.dot_general(
        select_grad, activated, contract_rows, preferred_element_type=jnp.float32
    )
    decay_log_grad = decay_grad * decay_mat
    conv_grad = act_total * silu_slope(convolved)
    conv_bias_grad = jnp.sum(conv_grad, axis=0)
    tap_grads = []
    ext_grad = jnp.zeros(extended.shape, jnp.float32)
    for tap_index in range(tap_count):
        masked = conv_grad * masks[tap_index]
        tap_grads.append(jnp.sum(masked * extended[tap_index : tap_index + row_count], axis=0))
        ext_grad = ext_grad.at[tap_index : tap_index + row_count].add(
            conv_weight[tap_index] * masked
        )
    conv_weight_grad = jnp.stack(tap_grads)
    from_next = passed_along(ext_grad[:lag_rows], "wide", -1)
    inner_grad = jnp.concatenate(
        [ext_grad[lag_rows:row_count], ext_grad[row_count:] + from_next], axis=0
    ).astype(jnp.bfloat16)
    projected_grad = jnp.stack([inner_grad, gate_grad], axis=1)
    normed_part = jnp.einsum(
        "tce,dce->td", projected_grad, in_weight, preferred_element_type=jnp.float32
    )
    normed_grad = lax.psum(normed_part, "narrow")
    scaled = normed_grad * norm_gain
    norm_gain_grad = jnp.sum(normed_grad * whole * inverse, axis=0)
    whole_grad = inverse * scaled - whole * (inverse * inverse * inverse) * jnp.mean(
        scaled * whole, axis=1, keepdims=True
    )
    width_mine = tokens.shape[1]
    mine = lax.dynamic_slice_in_dim(
        whole_grad, lax.axis_index("narrow") * width_mine, width_mine, 1
    )
    tokens_grad = (mine + cotangent.astype(jnp.float32)).astype(jnp.bfloat16)
    in_weight_grad = jnp.einsum(
        "td,tce->dce", normed, projected_grad, preferred_element_type=jnp.float32
    )
    summed_grads = lax.psum(
        (
            in_weight_grad,
            out_weight_grad,
            conv_weight_grad,
            conv_bias_grad,
            select_weight_grad,
            step_weight_grad,
            step_bias_grad,
            decay_log_grad,
            skip_gain_grad,
            norm_gain_grad,
        ),
        "wide",
    )
    (
        in_weight_grad,
        out_weight_grad,
        conv_weight_grad,
        conv_bias_grad,
        select_weight_grad,
        step_weight_grad,
        step_bias_grad,
        decay_log_grad,
        skip_gain_grad,
        norm_gain_grad,
    ) = summed_grads
    return (
        layer_out,
        tokens_grad,
        norm_gain_grad,
        in_weight_grad,
        conv_weight_grad,
        conv_bias_grad,
        select_weight_grad,
        step_weight_grad,
        step_bias_grad,
        decay_log_grad,
        skip_gain_grad,
        out_weight_grad,
    )


def solution(mesh):
    placed = (
        P("wide", "narrow"),
        P(),
        P(None, None, "narrow"),
        P(None, "narrow"),
        P("narrow"),
        P(None, "narrow"),
        P(None, "narrow"),
        P("narrow"),
        P(None, "narrow"),
        P("narrow"),
        P("narrow", None),
        P("wide"),
        P("wide", "narrow"),
    )
    return jax.shard_map(
        local,
        mesh=mesh,
        in_specs=placed,
        out_specs=(
            P("wide", "narrow"),
            P("wide", "narrow"),
            P(),
            P(None, None, "narrow"),
            P(None, "narrow"),
            P("narrow"),
            P(None, "narrow"),
            P(None, "narrow"),
            P("narrow"),
            P(None, "narrow"),
            P("narrow"),
            P("narrow", None),
        ),
        check_vma=False,
    )
```

profile of v0, /device:TPU:0, one launch (start us, length us, event | category | flops | bytes accessed | tf_op | source)
XLA Modules:
  0.0 2663.7 jit_solution(7222853000791807182)
XLA Ops:
  7.2 10.3 all_gather.36
  28.3 8.9 all_gather.43
  43.8 6.7 all_gather.38
  53.2 12.2 all-gather.8.cloned.1.call-done
  72.1 204.1 %while.230 = (s32[]{:T(128)}, f32[16,1024]{1,0:T(8,128)S(1)}, f32[4,64,1024]{2,1,0:T(8,128)}, f32[4,64,1024]{2,1,0:T(8,128)}, f32[4,64,16]{2,1,0:T(8,128)}, /*in...) while((s32[]{:T(128)}, f32[16,1024]{1,0:T(8,128)S(1)}, ...), condition=%wide.region_6.7_spmd, body=%wide.region_3.6_spmd.sunk | while | flops 663563 | bytes 1552618 | solution.py:86
  74.7 48.4 %while.240 = (s32[]{:T(128)}, f32[16,1024]{1,0:T(8,128)S(1)}, f32[8,8,1024]{2,1,0:T(8,128)S(1)}, f32[16,1024]{1,0:T(8,128)S(1)}, f32[8,8]{1,0:T(8,128)S(1)}, /*i...) while((s32[]{:T(128)}, f32[16,1024]{1,0:T(8,128)S(1)}, ...), condition=%wide.region_5.5_spmd, body=%wide.region_4.4_spmd.sunk | while | flops 663561 | bytes 494513 | solution.py:83
  125.8 48.4 %while.240 = (s32[]{:T(128)}, f32[16,1024]{1,0:T(8,128)S(1)}, f32[8,8,1024]{2,1,0:T(8,128)S(1)}, f32[16,1024]{1,0:T(8,128)S(1)}, f32[8,8]{1,0:T(8,128)S(1)}, /*i...) while((s32[]{:T(128)}, f32[16,1024]{1,0:T(8,128)S(1)}, ...), condition=%wide.region_5.5_spmd, body=%wide.region_4.4_spmd.sunk | while | flops 663561 | bytes 494513 | solution.py:83
  176.8 48.4 %while.240 = (s32[]{:T(128)}, f32[16,1024]{1,0:T(8,128)S(1)}, f32[8,8,1024]{2,1,0:T(8,128)S(1)}, f32[16,1024]{1,0:T(8,128)S(1)}, f32[8,8]{1,0:T(8,128)S(1)}, /*i...) while((s32[]{:T(128)}, f32[16,1024]{1,0:T(8,128)S(1)}, ...), condition=%wide.region_5.5_spmd, body=%wide.region_4.4_spmd.sunk | while | flops 663561 | bytes 494513 | solution.py:83
  227.8 48.4 %while.240 = (s32[]{:T(128)}, f32[16,1024]{1,0:T(8,128)S(1)}, f32[8,8,1024]{2,1,0:T(8,128)S(1)}, f32[16,1024]{1,0:T(8,128)S(1)}, f32[8,8]{1,0:T(8,128)S(1)}, /*i...) while((s32[]{:T(128)}, f32[16,1024]{1,0:T(8,128)S(1)}, ...), condition=%wide.region_5.5_spmd, body=%wide.region_4.4_spmd.sunk | while | flops 663561 | bytes 494513 | solution.py:83
  276.9 198.3 %while.235 = (s32[]{:T(128)}, f32[16,1024]{1,0:T(8,128)S(1)}, f32[4,64,1024]{2,1,0:T(8,128)}, f32[4,64,16]{2,1,0:T(8,128)}, f32[4,64]{1,0:T(4,128)}, /*index=5*/...) while((s32[]{:T(128)}, f32[16,1024]{1,0:T(8,128)S(1)}, ...), condition=%wide.region_25.26_spmd, body=%wide.region_22.25_spmd.sunk | while | flops 655373 | bytes 1454370 | solution.py:134
  279.5 46.9 %while.242 = (s32[]{:T(128)}, f32[16,1024]{1,0:T(8,128)S(1)}, f32[8,8,1024]{2,1,0:T(8,128)S(1)}, f32[16,1024]{1,0:T(8,128)S(1)}, f32[8,8]{1,0:T(8,128)S(1)}, /*i...) while((s32[]{:T(128)}, f32[16,1024]{1,0:T(8,128)S(1)}, ...), condition=%wide.region_24.24_spmd, body=%wide.region_23.23_spmd.sunk | while | flops 655370 | bytes 396229 | solution.py:128
  329.1 46.9 %while.242 = (s32[]{:T(128)}, f32[16,1024]{1,0:T(8,128)S(1)}, f32[8,8,1024]{2,1,0:T(8,128)S(1)}, f32[16,1024]{1,0:T(8,128)S(1)}, f32[8,8]{1,0:T(8,128)S(1)}, /*i...) while((s32[]{:T(128)}, f32[16,1024]{1,0:T(8,128)S(1)}, ...), condition=%wide.region_24.24_spmd, body=%wide.region_23.23_spmd.sunk | while | flops 655370 | bytes 396229 | solution.py:128
  378.7 46.9 %while.242 = (s32[]{:T(128)}, f32[16,1024]{1,0:T(8,128)S(1)}, f32[8,8,1024]{2,1,0:T(8,128)S(1)}, f32[16,1024]{1,0:T(8,128)S(1)}, f32[8,8]{1,0:T(8,128)S(1)}, /*i...) while((s32[]{:T(128)}, f32[16,1024]{1,0:T(8,128)S(1)}, ...), condition=%wide.region_24.24_spmd, body=%wide.region_23.23_spmd.sunk | while | flops 655370 | bytes 396229 | solution.py:128
  428.3 46.9 %while.242 = (s32[]{:T(128)}, f32[16,1024]{1,0:T(8,128)S(1)}, f32[8,8,1024]{2,1,0:T(8,128)S(1)}, f32[16,1024]{1,0:T(8,128)S(1)}, f32[8,8]{1,0:T(8,128)S(1)}, /*i...) while((s32[]{:T(128)}, f32[16,1024]{1,0:T(8,128)S(1)}, ...), condition=%wide.region_24.24_spmd, body=%wide.region_23.23_spmd.sunk | while | flops 655370 | bytes 396229 | solution.py:128
  475.2 22.9 all-gather.2
  498.1 18.9 all-gather.3
  518.0 34.6 %all-gather.12.cloned.1.call-done = f32[256,1024]{1,0:T(8,128)} async-done(((f32[16,1024]{1,0:T(8,128)}), f32[256,1024]{1,0:T(8,128)}) %all-gather.12.cloned.1.call-update) | async-done | bytes 1048592 | tf_op jit(solution)/shard_map/all_gather | solution.py:19
  553.7 305.0 %while.233 = (s32[]{:T(128)}, f32[16,1024]{1,0:T(8,128)S(1)}, f32[4,16,1024]{2,1,0:T(8,128)}, f32[4,64,1024]{2,1,0:T(8,128)}, f32[4,64,1024]{2,1,0:T(8,128)}, /*...) while((s32[]{:T(128)}, f32[16,1024]{1,0:T(8,128)S(1)}, ...), condition=%wide.region_20.21_spmd, body=%wide.region_9.20_spmd.sunk | while | flops 1245195 | bytes 3530806 | solution.py:106
  556.3 72.2 %while.241 = (s32[]{:T(128)}, f32[16,1024]{1,0:T(8,128)S(1)}, f32[8,8,1024]{2,1,0:T(8,128)S(1)}, f32[8,8,1024]{2,1,0:T(8,128)S(1)}, f32[16,1024]{1,0:T(8,128)S(1...) while((s32[]{:T(128)}, f32[16,1024]{1,0:T(8,128)S(1)}, ...), condition=%wide.region_19.19_spmd, body=%wide.region_10.18_spmd.sunk | while | flops 1245193 | bytes 1545941 | solution.py:103
  632.6 72.2 %while.241 = (s32[]{:T(128)}, f32[16,1024]{1,0:T(8,128)S(1)}, f32[8,8,1024]{2,1,0:T(8,128)S(1)}, f32[8,8,1024]{2,1,0:T(8,128)S(1)}, f32[16,1024]{1,0:T(8,128)S(1...) while((s32[]{:T(128)}, f32[16,1024]{1,0:T(8,128)S(1)}, ...), condition=%wide.region_19.19_spmd, body=%wide.region_10.18_spmd.sunk | while | flops 1245193 | bytes 1545941 | solution.py:103
  708.8 72.2 %while.241 = (s32[]{:T(128)}, f32[16,1024]{1,0:T(8,128)S(1)}, f32[8,8,1024]{2,1,0:T(8,128)S(1)}, f32[8,8,1024]{2,1,0:T(8,128)S(1)}, f32[16,1024]{1,0:T(8,128)S(1...) while((s32[]{:T(128)}, f32[16,1024]{1,0:T(8,128)S(1)}, ...), condition=%wide.region_19.19_spmd, body=%wide.region_10.18_spmd.sunk | while | flops 1245193 | bytes 1545941 | solution.py:103
  785.1 72.2 %while.241 = (s32[]{:T(128)}, f32[16,1024]{1,0:T(8,128)S(1)}, f32[8,8,1024]{2,1,0:T(8,128)S(1)}, f32[8,8,1024]{2,1,0:T(8,128)S(1)}, f32[16,1024]{1,0:T(8,128)S(1...) while((s32[]{:T(128)}, f32[16,1024]{1,0:T(8,128)S(1)}, ...), condition=%wide.region_19.19_spmd, body=%wide.region_10.18_spmd.sunk | while | flops 1245193 | bytes 1545941 | solution.py:103
  862.3 1407.1 %while.238 = (s32[]{:T(128)}, f32[16,1024]{1,0:T(8,128)S(1)}, f32[16,1024]{1,0:T(8,128)S(1)}, f32[4,64,1024]{2,1,0:T(8,128)}, f32[4,64,1024]{2,1,0:T(8,128)}, /*...) while((s32[]{:T(128)}, f32[16,1024]{1,0:T(8,128)S(1)}, ...), condition=%wide.region_65.66_spmd, body=%wide.region_28.65_spmd.sunk | while | flops 4562709 | bytes 13038639 | solution.py:182
  867.8 91.5 %while.243 = (s32[]{:T(128)}, f32[16,1024]{1,0:T(8,128)S(1)}, f32[8,8,16,1024]{3,2,1,0:T(8,128)}, f32[8,8,16,1024]{3,2,1,0:T(8,128)}, f32[8,8,1024]{2,1,0:T(8,12...) while((s32[]{:T(128)}, f32[16,1024]{1,0:T(8,128)S(1)}, ...), condition=%wide.region_30.30_spmd, body=%wide.region_29.29_spmd.sunk | while | flops 991240 | bytes 5055473 | solution.py:169
  964.3 246.5 %while.244 = (s32[]{:T(128)}, f32[16,1024]{1,0:T(8,128)S(1)}, f32[16,1024]{1,0:T(8,128)S(1)}, f32[8,8,1024]{2,1,0:T(8,128)S(1)}, f32[8,8,1024]{2,1,0:T(8,128)}, ...) while((s32[]{:T(128)}, f32[16,1024]{1,0:T(8,128)S(1)}, ...), condition=%wide.region_64.64_spmd, body=%wide.region_31.63_spmd.sunk | while | flops 3571466 | bytes 4548937 | solution.py:172
  988.8 6.3 multiply_add_fusion.43
  1019.8 6.3 multiply_add_fusion.43
  1050.6 6.3 multiply_add_fusion.43
  1081.4 6.3 multiply_add_fusion.43
  1112.2 6.3 multiply_add_fusion.43
  1143.0 6.3 multiply_add_fusion.43
  1173.8 6.3 multiply_add_fusion.43
  1204.6 6.3 multiply_add_fusion.43
  1219.6 91.5 %while.243 = (s32[]{:T(128)}, f32[16,1024]{1,0:T(8,128)S(1)}, f32[8,8,16,1024]{3,2,1,0:T(8,128)}, f32[8,8,16,1024]{3,2,1,0:T(8,128)}, f32[8,8,1024]{2,1,0:T(8,12...) while((s32[]{:T(128)}, f32[16,1024]{1,0:T(8,128)S(1)}, ...), condition=%wide.region_30.30_spmd, body=%wide.region_29.29_spmd.sunk | while | flops 991240 | bytes 5055473 | solution.py:169
  1316.1 246.5 %while.244 = (s32[]{:T(128)}, f32[16,1024]{1,0:T(8,128)S(1)}, f32[16,1024]{1,0:T(8,128)S(1)}, f32[8,8,1024]{2,1,0:T(8,128)S(1)}, f32[8,8,1024]{2,1,0:T(8,128)}, ...) while((s32[]{:T(128)}, f32[16,1024]{1,0:T(8,128)S(1)}, ...), condition=%wide.region_64.64_spmd, body=%wide.region_31.63_spmd.sunk | while | flops 3571466 | bytes 4548937 | solution.py:172
  1340.6 6.3 multiply_add_fusion.43
  1371.6 6.3 multiply_add_fusion.43
  1402.4 6.3 multiply_add_fusion.43
  1433.1 6.3 multiply_add_fusion.43
  1463.9 6.3 multiply_add_fusion.43
  1494.7 6.3 multiply_add_fusion.43
  1525.5 6.3 multiply_add_fusion.43
  1556.3 6.3 multiply_add_fusion.43
  1571.4 91.5 %while.243 = (s32[]{:T(128)}, f32[16,1024]{1,0:T(8,128)S(1)}, f32[8,8,16,1024]{3,2,1,0:T(8,128)}, f32[8,8,16,1024]{3,2,1,0:T(8,128)}, f32[8,8,1024]{2,1,0:T(8,12...) while((s32[]{:T(128)}, f32[16,1024]{1,0:T(8,128)S(1)}, ...), condition=%wide.region_30.30_spmd, body=%wide.region_29.29_spmd.sunk | while | flops 991240 | bytes 5055473 | solution.py:169
  1667.9 246.5 %while.244 = (s32[]{:T(128)}, f32[16,1024]{1,0:T(8,128)S(1)}, f32[16,1024]{1,0:T(8,128)S(1)}, f32[8,8,1024]{2,1,0:T(8,128)S(1)}, f32[8,8,1024]{2,1,0:T(8,128)}, ...) while((s32[]{:T(128)}, f32[16,1024]{1,0:T(8,128)S(1)}, ...), condition=%wide.region_64.64_spmd, body=%wide.region_31.63_spmd.sunk | while | flops 3571466 | bytes 4548937 | solution.py:172
  1692.4 6.3 multiply_add_fusion.43
  1723.3 6.3 multiply_add_fusion.43
  1754.1 6.3 multiply_add_fusion.43
  1784.9 6.3 multiply_add_fusion.43
  1815.7 6.3 multiply_add_fusion.43
  1846.5 6.3 multiply_add_fusion.43
  1877.3 6.3 multiply_add_fusion.43
  1908.1 6.3 multiply_add_fusion.43
  1923.1 91.5 %while.243 = (s32[]{:T(128)}, f32[16,1024]{1,0:T(8,128)S(1)}, f32[8,8,16,1024]{3,2,1,0:T(8,128)}, f32[8,8,16,1024]{3,2,1,0:T(8,128)}, f32[8,8,1024]{2,1,0:T(8,12...) while((s32[]{:T(128)}, f32[16,1024]{1,0:T(8,128)S(1)}, ...), condition=%wide.region_30.30_spmd, body=%wide.region_29.29_spmd.sunk | while | flops 991240 | bytes 5055473 | solution.py:169
  2019.6 246.5 %while.244 = (s32[]{:T(128)}, f32[16,1024]{1,0:T(8,128)S(1)}, f32[16,1024]{1,0:T(8,128)S(1)}, f32[8,8,1024]{2,1,0:T(8,128)S(1)}, f32[8,8,1024]{2,1,0:T(8,128)}, ...) while((s32[]{:T(128)}, f32[16,1024]{1,0:T(8,128)S(1)}, ...), condition=%wide.region_64.64_spmd, body=%wide.region_31.63_spmd.sunk | while | flops 3571466 | bytes 4548937 | solution.py:172
  2044.1 6.3 multiply_add_fusion.43
  2075.1 6.3 multiply_add_fusion.43
  2105.9 6.3 multiply_add_fusion.43
  2136.7 6.3 multiply_add_fusion.43
  2275.3 9.6 psum.84
  2324.8 36.5 %all-reduce.6.cloned.1.call-done = f32[256,1024]{1,0:T(8,128)} async-done(((f32[256,1024]{1,0:T(8,128)}), f32[256,1024]{1,0:T(8,128)}) %all-reduce.6.cloned.1.call-update) | async-done | bytes 1048592 | tf_op jit(solution)/shard_map/psum | solution.py:346
  2363.7 63.5 %all-reduce.1 = (f32[1024]{0:T(1024)}, f32[4,1024]{1,0:T(4,128)}, f32[1024]{0:T(1024)}, f32[1024]{0:T(1024)}, f32[1024]{0:T(1024)}) all-reduce(f32[1024]{0:T(1024)S(1)} %get-tuple-element.1569, f32[4,1024]{1,0:T(4,128)S(1)} %pad_maximum_fusion.5, f32[1024]{0:T(1024)S(1)} %get-tuple-element.1567, ...), channel_id=1, replica_groups=mesh['wide'=16,'narrow'=2] {'wide'}, use_global_device_ids=true, to_apply=%region_70.71 | all-reduce | flops 8192 | bytes 65536 | tf_op jit(solution)/shard_map/psum | solution.py:360
  2431.1 206.1 %all-reduce.8.cloned.1.call-done = (f32[1024,2,1024]{2,0,1:T(8,128)}, f32[96,1024]{1,0:T(8,128)}, f32[64,1024]{1,0:T(8,128)}, f32[16,1024]{1,0:T(8,128)}, f32[1024,1024]{1,0:T(8,128)}) async-done(((f32[1024,2,1024]{2,0,1:T(8,128)}, f32[96,1024]{1,0:T(8,128)}, f32[64,1024]{1,0:T(8,128)}, f32[16,1024]{1,0:T(8,128)}, f32[1024,1024]{1,0:T(8,128)}), (f32[1024,2,1024]{2,0,1:T(8,128)}, f32[96,1024]{1,0:T(8,128)}, ...) | async-done | bytes 13303824 | tf_op jit(solution)/shard_map/psum | solution.py:360
  2637.2 15.5 copy.36
  (3843 shorter events, 2008.5 us)
Async XLA Ops:
  7.2 32.1 %copy-start = (bf16[1024,1024]{1,0:T(8,128)(2,1)S(1)}, bf16[1024,1024]{1,0:T(8,128)(2,1)}, u32[]{:S(2)}) copy-start(bf16[1024,1024]{1,0:T(8,128)(2,1)} %param.53) | copy-start | bytes 6291460
  7.2 58.3 %all-gather.8.cloned.1.call-start = ((), (), s32[]{:S(2)}) async-start(), calls=%async_computation.1 | async-start | bytes 1572864 | tf_op jit(solution)/shard_map/all_gather | solution.py:259
  17.6 4.7 copy-start.2
  18.4 4.0 copy-start.30
  18.4 5.5 copy-start.46
  18.4 9.8 copy-start.38
  18.4 9.9 copy-start.17
  18.4 20.9 copy-start.55
  22.3 21.2 copy-start.11
  22.5 21.0 copy-start.10
  22.5 16.7 collective-permute-start
  23.9 13.3 collective-permute-start.1
  28.2 15.3 copy-start.34
  28.3 15.3 copy-start.36
  28.3 15.3 copy-start.39
  28.3 15.3 copy-start.48
  37.2 6.4 copy-start.14
  39.2 4.3 copy-start.41
  39.2 4.3 copy-start.43
  39.2 4.4 copy-start.50
  39.2 4.4 copy-start.52
  39.2 4.4 copy-start.32
  39.3 4.5 copy-start.26
  43.6 25.1 copy-start.27
  43.6 25.1 copy-start.56
  43.6 27.2 %copy-start.23 = (f32[16,1024]{1,0:T(8,128)S(1)}, f32[16,1024]{1,0:T(8,128)}, u32[]{:S(2)}) copy-start(f32[16,1024]{1,0:T(8,128)} %param.51) | copy-start | bytes 196612
  43.7 474.3 %all-gather.10.cloned.1.call-start = ((), (), s32[]{:S(2)}) async-start(), calls=%async_computation.4 | async-start | bytes 1114112 | tf_op jit(solution)/shard_map/all_gather | solution.py:19
  67.2 5.0 copy-start.21
  276.8 275.7 %all-gather.12.cloned.1.call-start = ((), (), s32[]{:S(2)}) async-start(), calls=%async_computation.5 | async-start | bytes 1114112 | tf_op jit(solution)/shard_map/all_gather | solution.py:19
  517.0 1844.3 %all-reduce.6.cloned.1.call-start = ((), (), s32[]{:S(2)}) async-start(), calls=%async_computation.3 | async-start | bytes 2097152 | tf_op jit(solution)/shard_map/psum | solution.py:346
  2269.3 15.5 copy-start.4
  2272.1 16.7 copy-start.49
  2272.1 16.7 copy-start.51
  2284.8 4.0 copy-start.57
  2288.7 1.6 copy-start.37
  2288.8 1.6 copy-start.42
  2290.3 1.3 copy-start.5
  2290.3 4.5 copy-start.35
  2290.3 4.5 copy-start.44
  2291.7 10.2 copy-start.33
  2291.7 10.2 copy-start.40
  2291.7 10.2 copy-start.53
  2300.3 6.3 copy-start.12
  2300.3 6.3 copy-start.54
  2300.4 5.5 collective-permute-start.2
  2306.7 2.7 copy-start.7
  2309.3 1.9 copy-start.24
  2309.3 2.6 copy-start.22
  2309.3 4.5 copy-start.6
  2309.3 120.0 %reduce-scatter.2.cloned.1.call-start = ((), (), s32[]{:S(2)}) async-start(), calls=%async_computation.2 | async-start | bytes 1572864 | tf_op jit(solution)/shard_map/reduce_scatter | solution.py:283
  2311.2 326.0 %all-reduce.8.cloned.1.call-start = ((), (), s32[]{:S(2)}) async-start(), calls=%async_computation.6 | async-start | bytes 26607616 | tf_op jit(solution)/shard_map/psum | solution.py:360
  2314.8 3.9 copy-start.3
  2314.8 3.9 copy-start.13
  2314.8 3.9 copy-start.16
  2314.8 3.9 copy-start.28
  2314.9 4.0 copy-start.31
  2323.6 40.1 %copy-start.47 = (f32[1024]{0:T(1024)S(1)}, f32[1024]{0:T(1024)}, u32[]{:S(2)}) copy-start(f32[1024]{0:T(1024)} %get-tuple-element.1794) | copy-start | bytes 12292
  2323.6 103.6 %copy-start.18 = (bf16[256,512]{1,0:T(8,128)(2,1)S(1)}, bf16[256,512]{1,0:T(8,128)(2,1)}, u32[]{:S(2)}) copy-start(bf16[256,512]{1,0:T(8,128)(2,1)} %param.55) | copy-start | bytes 786436
  2323.6 103.6 %copy-start.45 = (f32[256]{0:T(256)S(1)}, f32[256]{0:T(256)}, u32[]{:S(2)}) copy-start(f32[256]{0:T(256)} %get-tuple-element.2076) | copy-start | bytes 3076
  2323.6 105.7 %copy-start.19 = (bf16[256,512]{1,0:T(8,128)(2,1)S(1)}, bf16[256,512]{1,0:T(8,128)(2,1)}, u32[]{:S(2)}) copy-start(bf16[256,512]{1,0:T(8,128)(2,1)} %param.43) | copy-start | bytes 786436
  2637.2 15.5 copy-start.20
  2637.2 16.3 copy-start.25
  2637.2 17.0 copy-start.29
  2637.2 17.6 copy-start.9
  (3 other events, 2.2 us)
Sparse Core Ops, SparseCore 0:
  43.8 21.6 all-gather.7
  277.0 37.9 all-gather.9
  517.1 35.4 all-gather.11
  2309.5 51.7 all-reduce.5
  2363.5 20.3 reduce-scatter.1
  2389.8 247.3 all-reduce.7
where the time goes:
time: 2700 us; the launch traced here: 2660 us
  other arithmetic  1640 us (61%)
  local copies, waits for them, and re-layouts  523 us (19%)
  waiting for transfers between devices  290 us (11%)
  blocking collectives  141 us (5%)
  matrix products  30.7 us (1%)
    reduce_sum x96, other arithmetic, backward_row(): step_out = weighted * act_row + jnp.sum(held * decay_mat, axis=0)  384 us
    reduce_sum x160, other arithmetic, read_inner_row(): return (current, jnp.sum(read_row[:, None] * current, axis=0))  256 us
    psum x1, waiting for transfers between devices, local(): lax.psum((in_weight_grad, out_weight_grad, conv_weight_grad, conv_bias_gr...  206 us
    add x32, other arithmetic, backward_row(): decay_grad = decay_grad + held * step_row[None, :]  200 us
    while x192, other arithmetic  196 us
    add x32, other arithmetic, row_update(): return factor * current + in_row[:, None] * (step_row * act_row)[None, :]  164 us
    mul x32, other arithmetic, start_inner_row(): return (jnp.exp(step_row[None, :] * decay_mat) * keep_row * summed, None)  161 us
    dynamic_slice x352, local copies, waits for them, and re-layouts, final_advance(): lax.scan(final_inner_row, current, pieces, unroll=unroll_rows)  111 us
  transfers between devices with their start and end apart: 9, of which 4 were waited for; matrix products, arithmetic and copies ran while one was open for 9% of the time, Pallas kernels for 0%

commit v1 on v0

v1 whole, which is shorter than its diff:
```python
import functools

import jax
import jax.numpy as jnp
from jax import lax
from jax.experimental import pallas as pl
from jax.experimental.pallas import tpu as pltpu
from jax.sharding import PartitionSpec as P

epsilon = 1e-05
log2e = 1.4426950408889634
reset_step = 1e30
lanes = 128
body_rows = 32
scan_width = 512
vmem_bytes = 56 * 1024 * 1024
f32 = jnp.float32


def passed_along(array, axis, by):
    peers = lax.axis_size(axis)
    pairs = [(i, i + by) for i in range(peers) if 0 <= i + by < peers]
    return lax.ppermute(array, axis, pairs)


def swapped(array, axis, bit):
    peers = lax.axis_size(axis)
    return lax.ppermute(array, axis, [(i, i ^ bit) for i in range(peers)])


def silu_of(values):
    return values * jax.nn.sigmoid(values)


def silu_slope(values):
    logistic = jax.nn.sigmoid(values)
    return logistic * (1.0 + values * (1.0 - logistic))


def coef_columns(coef_ref, block):
    per_tile = lanes // body_rows
    start = pl.multiple_of((block // per_tile) * lanes, lanes)
    tile = coef_ref[:, pl.ds(start, lanes)]
    back = body_rows * lax.rem(block, per_tile)
    return pltpu.roll(tile, lax.rem(lanes - back, lanes), 1)


def ends_kernel(held_step_ref, drive_ref, grad_ref, coef_ref, decay_ref, out_ref):
    rows = held_step_ref.shape[0]
    count = decay_ref.shape[0]
    decay2 = decay_ref[...]
    zero = jnp.zeros(decay2.shape, f32)

    def body(block, carried):
        state, product, adjoint = carried
        columns = coef_columns(coef_ref, block)
        for i in range(body_rows):
            row = pl.ds(block * body_rows + i, 1)
            factor = jnp.exp2(held_step_ref[row, :] * decay2)
            state = factor * state + columns[:count, i : i + 1] * drive_ref[row, :]
            product = factor * product
            adjoint = adjoint + product * (columns[count:, i : i + 1] * grad_ref[row, :])
        return state, product, adjoint

    state, product, adjoint = lax.fori_loop(0, rows // body_rows, body, (zero, zero + 1.0, zero))
    out_ref[:count, :] = state
    out_ref[count : 2 * count, :] = adjoint
    total = jnp.sum(held_step_ref[...], axis=0, keepdims=True)
    out_ref[2 * count :, :] = jnp.broadcast_to(total, (8, total.shape[1]))


def column_spec(rows, width):
    return pl.BlockSpec((rows, width), lambda j: (0, j))


def whole_spec(rows, width):
    return pl.BlockSpec((rows, width), lambda j: (0, 0))


def scan_ends(held_step, drive, grad, coef, decay2):
    rows, width = held_step.shape
    count = decay2.shape[0]
    return pl.pallas_call(
        ends_kernel,
        grid=(width // scan_width,),
        in_specs=[column_spec(rows, scan_width)] * 3
        + [whole_spec(2 * count, rows), column_spec(count, scan_width)],
        out_specs=column_spec(2 * count + 8, scan_width),
        out_shape=jax.ShapeDtypeStruct((2 * count + 8, width), f32),
        compiler_params=pltpu.CompilerParams(vmem_limit_bytes=vmem_bytes),
        name="scan_ends",
    )(held_step, drive, grad, coef, decay2)


def lane_tiles(values):
    return [values[:, k : k + lanes] for k in range(0, values.shape[1], lanes)]


def tree_sum(parts):
    while len(parts) > 1:
        odd = parts[len(parts) // 2 * 2 :]
        parts = [a + b for a, b in zip(parts[0::2], parts[1::2])] + odd
    return parts[0]


def keep_halves(scratch, i, values):
    for k, tile in enumerate(lane_tiles(values)):
        at = (k * body_rows + i) * 8
        scratch[at : at + 8, :] = tile[:8] + tile[8:]


def put_state_sums(scratch, out_ref, block):
    for group in range(body_rows // 8):
        row = pl.ds(pl.multiple_of(block * body_rows + group * 8, 8), 8)
        for k in range(out_ref.shape[1] // lanes):
            at = (k * body_rows + group * 8) * 8
            total = tree_sum([scratch[pl.ds(at + n, 8, stride=8), :] for n in range(8)])
            out_ref[row, k * lanes : (k + 1) * lanes] = total


def scan_kernel(
    held_step_ref,
    step_ref,
    drive_ref,
    grad_ref,
    coef_ref,
    decay2_ref,
    decay_ref,
    entry_ref,
    tail_ref,
    read_ref,
    weighted_ref,
    held_ref,
    in_sum_ref,
    read_sum_ref,
    decay_grad_ref,
    states,
    factors,
    halves,
    more_halves,
):
    rows = step_ref.shape[0]
    count = decay_ref.shape[0]
    blocks = rows // body_rows
    decay2 = decay2_ref[...]
    decay = decay_ref[...]
    states[:count, :] = entry_ref[...]

    @pl.when(pl.program_id(0) == 0)
    def _():
        in_sum_ref[...] = jnp.zeros(in_sum_ref.shape, f32)
        read_sum_ref[...] = jnp.zeros(read_sum_ref.shape, f32)

    def at_token(t):
        return pl.ds(pl.multiple_of(t * count, count), count)

    def forward(block, state):
        columns = coef_columns(coef_ref, block)
        for i in range(body_rows):
            t = block * body_rows + i
            row = pl.ds(t, 1)
            factor = jnp.exp2(held_step_ref[row, :] * decay2)
            state = factor * state + columns[:count, i : i + 1] * drive_ref[row, :]
            factors[at_token(t), :] = factor
            states[at_token(t + 1), :] = state
            keep_halves(halves, i, columns[count:, i : i + 1] * state)
        put_state_sums(halves, read_ref, block)
        return state

    lax.fori_loop(0, blocks, forward, entry_ref[...])

    def backward(k, carried):
        adjoint, decay_grad = carried
        block = blocks - 1 - k
        columns = coef_columns(coef_ref, block)
        for i in range(body_rows - 1, -1, -1):
            t = block * body_rows + i
            row = pl.ds(t, 1)
            grad = grad_ref[row, :]
            drive = drive_ref[row, :]
            summed = columns[count:, i : i + 1] * grad + adjoint
            read_sum_ref[at_token(t), :] += tree_sum(lane_tiles(grad * states[at_token(t + 1), :]))
            in_sum_ref[at_token(t), :] += tree_sum(lane_tiles(summed * drive))
            keep_halves(halves, i, summed * columns[:count, i : i + 1])
            adjoint = factors[at_token(t), :] * summed
            held = adjoint * states[at_token(t), :]
            decay_grad = decay_grad + held * step_ref[row, :]
            keep_halves(more_halves, i, held * decay)
        put_state_sums(halves, weighted_ref, block)
        put_state_sums(more_halves, held_ref, block)
        return adjoint, decay_grad

    ignored, decay_grad = lax.fori_loop(
        0, blocks, backward, (tail_ref[...], jnp.zeros(decay.shape, f32))
    )
    decay_grad_ref[...] = decay_grad


def scan_full(held_step, step, drive, grad, coef, decay2, decay, entry, tail):
    rows, width = step.shape
    count = decay.shape[0]
    half_rows = 8 * body_rows * (scan_width // lanes)
    return pl.pallas_call(
        scan_kernel,
        grid=(width // scan_width,),
        in_specs=[column_spec(rows, scan_width)] * 4
        + [whole_spec(2 * count, rows)]
        + [column_spec(count, scan_width)] * 4,
        out_specs=[column_spec(rows, scan_width)] * 3
        + [whole_spec(rows * count, lanes)] * 2
        + [column_spec(count, scan_width)],
        out_shape=[jax.ShapeDtypeStruct((rows, width), f32)] * 3
        + [jax.ShapeDtypeStruct((rows * count, lanes), f32)] * 2
        + [jax.ShapeDtypeStruct((count, width), f32)],
        scratch_shapes=[
            pltpu.VMEM(((rows + 1) * count, scan_width), f32),
            pltpu.VMEM((rows * count, scan_width), f32),
            pltpu.VMEM((half_rows, lanes), f32),
            pltpu.VMEM((half_rows, lanes), f32),
        ],
        compiler_params=pltpu.CompilerParams(vmem_limit_bytes=vmem_bytes),
        name="scan_full",
    )(held_step, step, drive, grad, coef, decay2, decay, entry, tail)


def carried(ends, decay):
    count = decay.shape[0]
    place = lax.axis_index("wide")

    def split(packed):
        return packed[:count], packed[count : 2 * count], packed[2 * count : 2 * count + 1]

    def through(total):
        return jnp.exp(decay * total)

    zero = jnp.zeros(decay.shape, f32)
    none = jnp.zeros((1, decay.shape[1]), f32)
    before, before_steps, after, after_steps = zero, none, zero, none
    packed = ends
    for bit in (1, 2):
        second = (place & bit) != 0
        own = split(packed)
        other = split(swapped(packed, "wide", bit))
        early = [jnp.where(second, b, a) for a, b in zip(own, other)]
        late = [jnp.where(second, a, b) for a, b in zip(own, other)]
        before = before + jnp.where(second, through(before_steps) * other[0], 0.0)
        before_steps = before_steps + jnp.where(second, other[2], 0.0)
        after = after + jnp.where(second, 0.0, through(after_steps) * other[1])
        after_steps = after_steps + jnp.where(second, 0.0, other[2])
        state = late[0] + through(late[2]) * early[0]
        adjoint = early[1] + through(early[2]) * late[1]
        packed = jnp.concatenate(
            [state, adjoint, jnp.broadcast_to(early[2] + late[2], (8, decay.shape[1]))]
        )
    from_before = passed_along(packed[:count], "wide", 4)
    from_after = passed_along(packed[count : 2 * count], "wide", -4)
    return (
        before + through(before_steps) * from_before,
        after + through(after_steps) * from_after,
    )


def local(
    tokens,
    norm_gain,
    in_weight,
    conv_weight,
    conv_bias,
    select_weight,
    step_weight,
    step_bias,
    decay_log,
    skip_gain,
    out_weight,
    segment_ids,
    cotangent,
):
    row_count = tokens.shape[0]
    tap_count = conv_weight.shape[0]
    lag_rows = tap_count - 1
    rank_size = step_weight.shape[0]
    state_count = decay_log.shape[0]
    contract_rows = (((0,), (0,)), ((), ()))
    contract_last = (((1,), (1,)), ((), ()))
    whole = lax.all_gather(tokens, "narrow", axis=1, tiled=True).astype(jnp.float32)
    inverse = lax.rsqrt(jnp.mean(whole * whole, axis=1, keepdims=True) + epsilon)
    normed = (whole * inverse * norm_gain).astype(jnp.bfloat16)
    projected = jnp.einsum(
        "td,dce->tce", normed, in_weight, preferred_element_type=jnp.float32
    ).astype(jnp.bfloat16)
    inner_half = projected[:, 0].astype(jnp.float32)
    gate_half = projected[:, 1].astype(jnp.float32)
    seg_float = segment_ids.astype(jnp.float32)
    prior_rows, prior_seg = passed_along(
        (inner_half[row_count - lag_rows :], seg_float[row_count - lag_rows :]), "wide", 1
    )
    extended = jnp.concatenate([prior_rows, inner_half], axis=0)
    ext_seg = jnp.concatenate([prior_seg, seg_float], axis=0)
    masks = []
    convolved = conv_bias + jnp.zeros(inner_half.shape, jnp.float32)
    for tap_index in range(tap_count):
        tap_mask = jnp.where(ext_seg[tap_index : tap_index + row_count] == seg_float, 1.0, 0.0)[
            :, None
        ]
        masks.append(tap_mask)
        convolved = (
            convolved
            + conv_weight[tap_index] * extended[tap_index : tap_index + row_count] * tap_mask
        )
    keep_flag = jnp.where(
        seg_float == jnp.concatenate([prior_seg[lag_rows - 1 :], seg_float[:-1]]), 1.0, 0.0
    )
    activated = silu_of(convolved).astype(jnp.bfloat16)
    act_float = activated.astype(jnp.float32)
    all_act, all_weight = (
        lax.all_gather(activated, "narrow", axis=1, tiled=True),
        lax.all_gather(select_weight, "narrow", axis=1, tiled=True),
    )
    selected = lax.dot_general(
        all_act, all_weight, contract_last, preferred_element_type=jnp.float32
    )
    step_low = selected[:, :rank_size].astype(jnp.bfloat16)
    step_pre = jnp.dot(step_low, step_weight, preferred_element_type=jnp.float32) + step_bias
    step_size = jax.nn.softplus(step_pre)
    decay_mat = -jnp.exp(decay_log)
    decay2 = decay_mat * log2e
    held_step = jnp.where(keep_flag[:, None] > 0.0, step_size, reset_step)
    drive = step_size * act_float
    coef = selected[:, rank_size:].T
    gate_act = silu_of(gate_half)
    cot_whole = lax.all_gather(cotangent, "narrow", axis=1, tiled=True)
    gated_grad = lax.dot_general(
        cot_whole, out_weight, contract_last, preferred_element_type=jnp.float32
    )
    scan_grad = gated_grad * gate_act
    ends = scan_ends(held_step, drive, scan_grad, coef, decay2)
    entry_state, tail_adjoint = carried(ends, decay_mat)
    scanned, weighted, held_sum, in_sum, read_sum, decay_grad = scan_full(
        held_step, step_size, drive, scan_grad, coef, decay2, decay_mat, entry_state, tail_adjoint
    )
    scanned = scanned + skip_gain * act_float
    gated = (scanned * gate_act).astype(jnp.bfloat16)
    out_part = jnp.dot(gated, out_weight, preferred_element_type=jnp.float32)
    out_mine = lax.psum_scatter(out_part, "narrow", scatter_dimension=1, tiled=True)
    layer_out = (tokens.astype(jnp.float32) + out_mine).astype(jnp.bfloat16)
    out_weight_grad = lax.dot_general(
        gated, cot_whole, contract_rows, preferred_element_type=jnp.float32
    )
    gate_grad = (gated_grad * scanned * silu_slope(gate_half)).astype(jnp.bfloat16)
    skip_gain_grad = jnp.sum(scan_grad * act_float, axis=0)
    step_grad = act_float * weighted + held_sum
    act_grad = step_size * weighted
    in_grad = jnp.sum(in_sum, axis=1).reshape(row_count, state_count)
    read_grad = jnp.sum(read_sum, axis=1).reshape(row_count, state_count)
    act_grad = act_grad + skip_gain * scan_grad
    pre_grad = (step_grad * jax.nn.sigmoid(step_pre)).astype(jnp.bfloat16)
    step_bias_grad = jnp.sum(pre_grad.astype(jnp.float32), axis=0)
    step_weight_grad = lax.dot_general(
        step_low, pre_grad, contract_rows, preferred_element_type=jnp.float32
    )
    low_grad = lax.dot_general(
        pre_grad, step_weight, contract_last, preferred_element_type=jnp.float32
    )
    select_grad = lax.psum(
        jnp.concatenate([low_grad, in_grad, read_grad], axis=1), "narrow"
    ).astype(jnp.bfloat16)
    act_total = act_grad + jnp.dot(select_grad, select_weight, preferred_element_type=jnp.float32)
    select_weight_grad = lax.dot_general(
        select_grad, activated, contract_rows, preferred_element_type=jnp.float32
    )
    decay_log_grad = decay_grad * decay_mat
    conv_grad = act_total * silu_slope(convolved)
    conv_bias_grad = jnp.sum(conv_grad, axis=0)
    tap_grads = []
    ext_grad = jnp.zeros(extended.shape, jnp.float32)
    for tap_index in range(tap_count):
        masked = conv_grad * masks[tap_index]
        tap_grads.append(jnp.sum(masked * extended[tap_index : tap_index + row_count], axis=0))
        ext_grad = ext_grad.at[tap_index : tap_index + row_count].add(
            conv_weight[tap_index] * masked
        )
    conv_weight_grad = jnp.stack(tap_grads)
    from_next = passed_along(ext_grad[:lag_rows], "wide", -1)
    inner_grad = jnp.concatenate(
        [ext_grad[lag_rows:row_count], ext_grad[row_count:] + from_next], axis=0
    ).astype(jnp.bfloat16)
    projected_grad = jnp.stack([inner_grad, gate_grad], axis=1)
    normed_part = jnp.einsum(
        "tce,dce->td", projected_grad, in_weight, preferred_element_type=jnp.float32
    )
    normed_grad = lax.psum(normed_part, "narrow")
    scaled = normed_grad * norm_gain
    norm_gain_grad = jnp.sum(normed_grad * whole * inverse, axis=0)
    whole_grad = inverse * scaled - whole * (inverse * inverse * inverse) * jnp.mean(
        scaled * whole, axis=1, keepdims=True
    )
    width_mine = tokens.shape[1]
    mine = lax.dynamic_slice_in_dim(
        whole_grad, lax.axis_index("narrow") * width_mine, width_mine, 1
    )
    tokens_grad = (mine + cotangent.astype(jnp.float32)).astype(jnp.bfloat16)
    in_weight_grad = jnp.einsum(
        "td,tce->dce", normed, projected_grad, preferred_element_type=jnp.float32
    )
    summed_grads = lax.psum(
        (
            in_weight_grad,
            out_weight_grad,
            conv_weight_grad,
            conv_bias_grad,
            select_weight_grad,
            step_weight_grad,
            step_bias_grad,
            decay_log_grad,
            skip_gain_grad,
            norm_gain_grad,
        ),
        "wide",
    )
    (
        in_weight_grad,
        out_weight_grad,
        conv_weight_grad,
        conv_bias_grad,
        select_weight_grad,
        step_weight_grad,
        step_bias_grad,
        decay_log_grad,
        skip_gain_grad,
        norm_gain_grad,
    ) = summed_grads
    return (
        layer_out,
        tokens_grad,
        norm_gain_grad,
        in_weight_grad,
        conv_weight_grad,
        conv_bias_grad,
        select_weight_grad,
        step_weight_grad,
        step_bias_grad,
        decay_log_grad,
        skip_gain_grad,
        out_weight_grad,
    )


def solution(mesh):
    placed = (
        P("wide", "narrow"),
        P(),
        P(None, None, "narrow"),
        P(None, "narrow"),
        P("narrow"),
        P(None, "narrow"),
        P(None, "narrow"),
        P("narrow"),
        P(None, "narrow"),
        P("narrow"),
        P("narrow", None),
        P("wide"),
        P("wide", "narrow"),
    )
    return jax.shard_map(
        local,
        mesh=mesh,
        in_specs=placed,
        out_specs=(
            P("wide", "narrow"),
            P("wide", "narrow"),
            P(),
            P(None, None, "narrow"),
            P(None, "narrow"),
            P("narrow"),
            P(None, "narrow"),
            P(None, "narrow"),
            P("narrow"),
            P(None, "narrow"),
            P("narrow"),
            P("narrow", None),
        ),
        check_vma=False,
    )
```

time: 2700 us -> 528 us (0.20); the launches traced: 2660 us -> 527 us
  other arithmetic: 1640 us -> 35.2 us
  local copies, waits for them, and re-layouts: 523 us -> 39.8 us
  blocking collectives: 141 us -> 101 us
  waiting for transfers between devices: 290 us -> 254 us
  Pallas kernels: 0 us -> 33.6 us
    reduce_sum x352 -> x2, other arithmetic: 796 us -> 5.02 us  [the longest x1 2.81 us: local(): read_grad = jnp.sum(read_sum, axis=1).reshape(row_count, state_count)]
    add x96 -> x5, other arithmetic: 365 us -> 5.17 us  [the longest x2 1.94 us: carried(): adjoint = early[1] + through(early[2]) * late[1]]
    while x192 -> x0, other arithmetic: 196 us -> none
    mul x1344 -> x1, other arithmetic: 192 us -> 0.65 us  [local(): decay2 = decay_mat * log2e]
    slice x417 -> x0, local copies, waits for them, and re-layouts: 155 us -> none  [the longest x128 60 us: scan_retreat(): lax.scan(backward_row, carried, (step_blk, act_blk, in_blk, read_blk, kee...]
    dynamic_slice x368 -> x0, local copies, waits for them, and re-layouts: 122 us -> none  [the longest x352 111 us: final_advance(): lax.scan(final_inner_row, current, pieces, unroll=unroll_rows)]
    dynamic_update_slice x144 -> x0, local copies, waits for them, and re-layouts: 92.6 us -> none  [the longest x32 34.8 us: scan_retreat(): lax.scan(forward_row, begin_state, (step_blk, act_blk, in_blk, keep_blk),...]
    concatenate x64 -> x1, other arithmetic: 61 us -> 0.68 us  [carried(): jnp.concatenate([state, adjoint, jnp.broadcast_to(early[2] + late[2], (8,...]
  transfers between devices with their start and end apart: 9 -> 11, of which waited for: 4 -> 7; matrix products, arithmetic and copies ran while one was open for 9% -> 6% of each run, Pallas kernels for 0% -> 0%
where the time goes in v1:
time: 528 us; the launch traced here: 527 us
  waiting for transfers between devices  254 us (48%)
  blocking collectives  101 us (19%)
  local copies, waits for them, and re-layouts  39.8 us (8%)
  other arithmetic  35.2 us (7%)
  Pallas kernels  33.6 us (6%)
  matrix products  33.2 us (6%)
  starting transfers between devices  14.4 us (3%)
  between operations  14.4 us (3%)
    psum x1, waiting for transfers between devices, local(): lax.psum((in_weight_grad, out_weight_grad, conv_weight_grad, conv_bias_gr...  208 us
    psum x1, blocking collectives, local(): lax.psum((in_weight_grad, out_weight_grad, conv_weight_grad, conv_bias_gr...  63.4 us
    psum x1, waiting for transfers between devices, local(): normed_grad = lax.psum(normed_part, 'narrow')  26.9 us
    pallas_call x1, Pallas kernels, scan_full(): pl.pallas_call(scan_kernel, grid=(width // scan_width,), in_specs=[column...  24.2 us
    unnamed x111, local copies, waits for them, and re-layouts  23.7 us
    ppermute x5, starting transfers between devices, passed_along(): return lax.ppermute(array, axis, pairs)  12.8 us
  transfers between devices with their start and end apart: 11, of which 7 were waited for; matrix products, arithmetic and copies ran while one was open for 6% of the time, Pallas kernels for 0%

profile of v1, /device:TPU:0, one launch (start us, length us, event | category | flops | bytes accessed | tf_op | source)
XLA Modules:
  0.0 526.6 jit_solution(6187993295324114702)
XLA Ops:
  7.2 0.8 convert_element_type.67
  8.1 2.3 collective-permute-start
  10.5 9.3 %all_gather.12 = bf16[256,1024]{1,0:T(8,128)(2,1)S(1)} all-gather(bf16[256,512]{1,0:T(8,128)(2,1)} %param.21), channel_id=1, replica_groups=mesh['wide'=16,'narrow'=2] {'narrow'}, dimensions={1}, use_global_device_ids=true | all-gather | bytes 786432 | tf_op jit(solution)/shard_map/all_gather | solution.py:285
  20.5 3.9 fusion.4
  24.8 3.0 collective-permute-start.1
  27.9 9.1 %all_gather.15 = bf16[256,1024]{1,0:T(8,128)(2,1)S(1)} all-gather(bf16[256,512]{1,0:T(8,128)(2,1)S(1)} %copy-done.16), channel_id=1, replica_groups=mesh['wide'=16,'narrow'=2] {'narrow'}, dimensions={1}, use_global_device_ids=true | all-gather | bytes 786432 | tf_op jit(solution)/shard_map/all_gather | solution.py:331
  37.2 4.2 fusion.24
  41.6 10.4 %all_gather.14 = bf16[96,2048]{1,0:T(8,128)(2,1)} all-gather(bf16[96,1024]{1,0:T(8,128)(2,1)} %param.26), channel_id=1, replica_groups=mesh['wide'=16,'narrow'=2] {'narrow'}, dimensions={1}, use_global_device_ids=true | all-gather | bytes 589824 | tf_op jit(solution)/shard_map/all_gather | solution.py:317
  53.2 0.7 fusion.45
  53.9 10.4 %all-gather.2.cloned.1.call-done = bf16[256,2048]{1,0:T(8,128)(2,1)} async-done(((bf16[256,1024]{1,0:T(8,128)(2,1)}), bf16[256,2048]{1,0:T(8,128)(2,1)}) %all-gather.2.cloned.1.call-update) | async-done | bytes 1048592 | tf_op jit(solution)/shard_map/all_gather | solution.py:316
  64.4 1.8 fusion.53
  66.8 3.8 convert_multiply_fusion.3
  70.6 9.4 %scan_ends.1 = f32[40,1024]{1,0:T(8,128)} custom-call(f32[256,1024]{1,0:T(8,128)} %get-tuple-element.131.held_step_ref, f32[256,1024]{1,0:T(8,128)} %get-tuple-element.130.drive_ref, f32[256,1024]{1,0:T(8,128)} %get-tuple-element.114.grad_ref, f32[32,256]{1,0:T(8,128)} %slice_bitcast_fusion.1.coef_ref, f32[16,1024]{1,0:T(8,128)} %broadcast_multiply_fusion.1.decay_ref.decay2_ref), custom_call_target="tpu_custom_call" | custom-call | tf_op jit(solution)/shard_map/scan_ends/pallas_call | solution.py:83
  80.0 1.7 collective-permute-done.2
  81.7 0.8 fusion.51
  82.5 1.0 multiply_add_fusion.6
  84.1 0.7 pad_maximum_fusion.4
  84.8 1.5 collective-permute-start.3
  86.3 5.1 collective-permute-done.3
  91.4 0.8 fusion.44
  92.2 1.0 multiply_add_fusion.3
  93.1 1.3 collective-permute-start.5
  94.4 4.5 collective-permute-start.4
  99.3 1.6 collective-permute-done.4
  100.9 1.6 multiply_add_fusion.2
  102.5 24.2 %scan_full.1 = (f32[256,1024]{1,0:T(8,128)}, f32[256,1024]{1,0:T(8,128)}, f32[256,1024]{1,0:T(8,128)}, f32[4096,128]{1,0:T(8,128)}, f32[4096,128]{1,0:T(8,128)}, /*index=5*/f32[16,1024]{1,0:T(8,128)}) custom-call(f32[256,1024]{1,0:T(8,128)} %get-tuple-element.131.held_step_ref, f32[256,1024]{1,0:T(8,128)} %get-tuple-element.132.step_ref, ...), custom_call_target="tpu_custom_call" | custom-call | tf_op jit(solution)/shard_map/scan_full/pallas_call | solution.py:203
  126.8 2.2 reduce_sum.109
  129.0 2.8 reduce_sum.110
  131.8 5.2 convert_reduce_fusion
  137.1 0.8 copy-done.5
  138.1 1.5 reshape.191
  139.6 1.6 copy.31
  141.2 0.8 reshape.190
  141.9 1.0 copy.30
  142.9 1.4 pad_maximum_fusion.5
  144.3 9.3 %psum.84 = bf16[256,96]{0,1:T(8,128)(2,1)S(1)} all-reduce(f32[256,96]{0,1:T(8,128)} %pad_maximum_fusion.5), channel_id=1, replica_groups=mesh['wide'=16,'narrow'=2] {'narrow'}, use_global_device_ids=true, to_apply=%region_4.5 | all-reduce | flops 24576 | bytes 147456 | tf_op jit(solution)/shard_map/psum | solution.py:364
  153.6 3.4 multiply_multiply_fusion
  157.1 1.2 scatter-add.10
  158.4 1.2 multiply_add_fusion
  159.6 4.0 scatter-add.11
  163.6 2.7 slice_add_fusion.1
  166.3 4.0 scatter-add.14
  170.3 0.8 slice.234
  171.1 1.5 collective-permute-start.6
  172.7 4.4 multiply_reduce_fusion.3
  177.2 0.8 copy-done.13
  178.0 2.7 fusion.7
  180.7 2.7 fusion.54
  183.5 1.6 fusion.48
  185.1 2.0 fusion.41
  187.1 1.0 fusion.57
  188.1 2.8 fusion.56
  190.9 4.8 fusion.32
  196.4 26.9 %all-reduce.6.cloned.1.call-done = f32[256,1024]{1,0:T(8,128)} async-done(((f32[256,1024]{1,0:T(8,128)}), f32[256,1024]{1,0:T(8,128)}) %all-reduce.6.cloned.1.call-update) | async-done | bytes 1048592 | tf_op jit(solution)/shard_map/psum | solution.py:391
  223.3 1.5 multiply_reduce_fusion.4
  224.8 63.4 %all-reduce.1 = (f32[1024]{0:T(1024)}, f32[4,1024]{1,0:T(4,128)}, f32[1024]{0:T(1024)}, f32[1024]{0:T(1024)}, f32[1024]{0:T(1024)}) all-reduce(f32[1024]{0:T(1024)S(1)} %get-tuple-element.101, f32[4,1024]{1,0:T(4,128)S(1)} %pad_maximum_fusion.6, f32[1024]{0:T(1024)S(1)} %get-tuple-element.99, ...), channel_id=1, replica_groups=mesh['wide'=16,'narrow'=2] {'wide'}, use_global_device_ids=true, to_apply=%region_8.9 | all-reduce | flops 8192 | bytes 65536 | tf_op jit(solution)/shard_map/psum | solution.py:405
  288.3 0.9 fusion.29
  289.2 1.8 add_convert_fusion
  291.0 208.3 %all-reduce.8.cloned.1.call-done = (f32[1024,2,1024]{2,0,1:T(8,128)}, f32[96,1024]{1,0:T(8,128)}, f32[64,1024]{1,0:T(8,128)}, f32[16,1024]{1,0:T(8,128)}, f32[1024,1024]{1,0:T(8,128)}) async-done(((f32[1024,2,1024]{2,0,1:T(8,128)}, f32[96,1024]{1,0:T(8,128)}, f32[64,1024]{1,0:T(8,128)}, f32[16,1024]{1,0:T(8,128)}, f32[1024,1024]{1,0:T(8,128)}), (f32[1024,2,1024]{2,0,1:T(8,128)}, f32[96,1024]{1,0:T(8,128)}, ...) | async-done | bytes 13303824 | tf_op jit(solution)/shard_map/psum | solution.py:405
  499.3 15.5 %copy.34 = f32[1024,2,1024]{2,1,0:T(2,128)} copy(f32[1024,2,1024]{2,0,1:T(8,128)} %get-tuple-element.108) | data formatting | bytes 16777216
  514.8 0.7 copy.53
  515.6 0.7 copy.54
  516.9 2.1 copy.56
  519.1 1.0 copy-done.1
  (136 shorter events, 6.2 us)
Async XLA Ops:
  7.2 30.0 %copy-start = (bf16[1024,1024]{1,0:T(8,128)(2,1)S(1)}, bf16[1024,1024]{1,0:T(8,128)(2,1)}, u32[]{:S(2)}) copy-start(bf16[1024,1024]{1,0:T(8,128)(2,1)} %param.31) | copy-start | bytes 6291460
  7.2 57.2 %all-gather.2.cloned.1.call-start = ((), (), s32[]{:S(2)}) async-start(), calls=%async_computation.1 | async-start | bytes 1572864 | tf_op jit(solution)/shard_map/all_gather | solution.py:316
  8.1 28.8 %collective-permute-start = (f32[3]{0:T(128)S(1)}, f32[3]{0:T(128)S(1)}, u32[]{:S(2)}, u32[]{:S(2)}) collective-permute-start(f32[3]{0:T(128)S(1)} %slice.178), channel_id=1, source_target_pairs={{0,2},{2,4},{4,6},{6,8},{8,10},{10,12},{12,14},{14,16},{16,18},{18... | collective-permute-start | bytes 44 | tf_op jit(solution)/shard_map/ppermute | solution.py:23
  20.5 3.9 copy-start.25
  24.4 17.0 %copy-start.8 = (bf16[256,2,1024]{2,0,1:T(8,128)(2,1)}, bf16[256,2,1024]{2,0,1:T(8,128)(2,1)S(1)}, u32[]{:S(2)}) copy-start(bf16[256,2,1024]{2,0,1:T(8,128)(2,1)S(1)} %fusion.4) | copy-start | bytes 3145732
  24.4 3.4 copy-start.34
  24.4 3.4 copy-start.16
  24.5 12.6 %copy-start.39 = (s32[256]{0:T(256)S(1)}, s32[256]{0:T(256)}, u32[]{:S(2)}) copy-start(s32[256]{0:T(256)} %param.32) | copy-start | bytes 3076
  24.5 12.7 %copy-start.52 = (f32[1024]{0:T(1024)S(1)}, f32[1024]{0:T(1024)}, u32[]{:S(2)}) copy-start(f32[1024]{0:T(1024)} %param.25) | copy-start | bytes 12292
  24.7 16.7 %copy-start.7 = (f32[256,1024]{1,0:T(8,128)}, f32[256,1024]{1,0:T(8,128)S(1)}, u32[]{:S(2)}) copy-start(f32[256,1024]{1,0:T(8,128)S(1)} %get-tuple-element.134) | copy-start | bytes 3145732
  24.8 12.4 %collective-permute-start.1 = (f32[3,1024]{1,0:T(4,128)S(1)}, f32[3,1024]{1,0:T(4,128)S(1)}, u32[]{:S(2)}, u32[]{:S(2)}) collective-permute-start(f32[3,1024]{1,0:T(4,128)S(1)} %slice_bitcast_fusion.2), channel_id=1, source_target_pairs={{0,2},{2,4},{4,6},{6,8},{8,10},{10,12},{12,14},{14,16},{16,18},{18... | collective-permute-start | bytes 36872 | tf_op jit(solution)/shard_map/ppermute | solution.py:23
  27.8 13.6 %copy-start.29 = (f32[1,1024]{1,0:T(1,128)}, f32[1,1024]{1,0:T(1,128)S(1)}, u32[]{:S(2)}) copy-start(f32[1,1024]{1,0:T(1,128)S(1)} %get-tuple-element.153) | copy-start | bytes 12292
  27.9 13.6 %copy-start.31 = (f32[1,1024]{1,0:T(1,128)}, f32[1,1024]{1,0:T(1,128)S(1)}, u32[]{:S(2)}) copy-start(f32[1,1024]{1,0:T(1,128)S(1)} %get-tuple-element.151) | copy-start | bytes 12292
  27.9 13.5 %copy-start.35 = (f32[1,1024]{1,0:T(1,128)}, f32[1,1024]{1,0:T(1,128)S(1)}, u32[]{:S(2)}) copy-start(f32[1,1024]{1,0:T(1,128)S(1)} %get-tuple-element.152) | copy-start | bytes 12292
  27.9 13.5 %copy-start.47 = (f32[1,1024]{1,0:T(1,128)}, f32[1,1024]{1,0:T(1,128)S(1)}, u32[]{:S(2)}) copy-start(f32[1,1024]{1,0:T(1,128)S(1)} %get-tuple-element.150) | copy-start | bytes 12292
  37.0 4.5 copy-start.11
  37.1 4.3 copy-start.40
  37.1 4.3 copy-start.42
  37.1 4.3 copy-start.49
  37.1 4.3 copy-start.50
  37.2 4.3 copy-start.27
  37.2 14.8 %copy-start.15 = (f32[16,1024]{1,0:T(8,128)S(1)}, f32[16,1024]{1,0:T(8,128)}, u32[]{:S(2)}) copy-start(f32[16,1024]{1,0:T(8,128)} %param.29) | copy-start | bytes 196612
  41.5 25.3 %copy-start.3 = (bf16[256,1024]{1,0:T(8,128)(2,1)S(1)}, bf16[256,1024]{1,0:T(8,128)(2,1)}, u32[]{:S(2)}) copy-start(bf16[256,1024]{1,0:T(8,128)(2,1)} %get-tuple-element.115) | copy-start | bytes 1572868
  41.5 25.3 %copy-start.48 = (f32[1024]{0:T(1024)S(1)}, f32[1024]{0:T(1024)}, u32[]{:S(2)}) copy-start(f32[1024]{0:T(1024)} %param.28) | copy-start | bytes 12292
  41.5 181.7 %all-reduce.6.cloned.1.call-start = ((), (), s32[]{:S(2)}) async-start(), calls=%async_computation.3 | async-start | bytes 2097152 | tf_op jit(solution)/shard_map/psum | solution.py:391
  66.2 4.5 copy-start.18
  80.0 1.7 collective-permute-start.2
  83.5 0.6 copy-start.19
  84.8 6.6 %collective-permute-start.3 = (f32[40,1024]{1,0:T(8,128)}, f32[40,1024]{1,0:T(8,128)}, u32[]{:S(2)}, u32[]{:S(2)}) collective-permute-start(f32[40,1024]{1,0:T(8,128)} %pad_maximum_fusion.4), channel_id=1, source_target_pairs={{0,4},{2,6},{4,0},{6,2},{8,12},{10,14},{12,8},{14,10},{16,20},{18,... | collective-permute-start | bytes 491528 | tf_op jit(solution)/shard_map/ppermute | solution.py:28
  93.1 6.2 %collective-permute-start.5 = (f32[16,1024]{1,0:T(8,128)S(1)}, f32[16,1024]{1,0:T(8,128)S(1)}, u32[]{:S(2)}, u32[]{:S(2)}) collective-permute-start(f32[16,1024]{1,0:T(8,128)S(1)} %get-tuple-element.143), channel_id=1, source_target_pairs={{8,0},{10,2},{12,4},{14,6},{16,8},{18,10},{20,12},{22,14},{24,16},... | collective-permute-start | bytes 196616 | tf_op jit(solution)/shard_map/ppermute | solution.py:23
  94.4 6.4 %collective-permute-start.4 = (f32[16,1024]{1,0:T(8,128)S(1)}, f32[16,1024]{1,0:T(8,128)S(1)}, u32[]{:S(2)}, u32[]{:S(2)}) collective-permute-start(f32[16,1024]{1,0:T(8,128)S(1)} %get-tuple-element.144), channel_id=1, source_target_pairs={{0,8},{2,10},{4,12},{6,14},{8,16},{10,18},{12,20},{14,22},{16,24},... | collective-permute-start | bytes 196616 | tf_op jit(solution)/shard_map/ppermute | solution.py:23
  126.8 5.0 copy-start.44
  131.8 6.0 %copy-start.20 = (bf16[64,1024]{1,0:T(8,128)(2,1)S(1)}, bf16[64,1024]{1,0:T(8,128)(2,1)}, u32[]{:S(2)}) copy-start(bf16[64,1024]{1,0:T(8,128)(2,1)} %param.27) | copy-start | bytes 393220
  137.1 0.8 copy-start.5
  157.0 1.3 copy-start.2
  157.1 1.3 copy-start.32
  157.1 1.3 copy-start.43
  158.4 5.2 copy-start.30
  158.4 5.2 copy-start.41
  163.6 9.1 %copy-start.28 = (f32[3,1024]{1,0:T(4,128)S(1)}, f32[3,1024]{1,0:T(4,128)}, u32[]{:S(2)}) copy-start(f32[3,1024]{1,0:T(4,128)} %copy-done.27) | copy-start | bytes 36868
  163.6 9.1 %copy-start.36 = (f32[1,1024]{1,0:T(1,128)S(1)}, f32[1,1024]{1,0:T(1,128)}, u32[]{:S(2)}) copy-start(f32[1,1024]{1,0:T(1,128)} %copy-done.35) | copy-start | bytes 12292
  171.1 6.9 %copy-start.9 = (bf16[256,1,1024]{2,0,1:T(8,128)(2,1)S(1)}, bf16[256,1,1024]{2,0,1:T(8,128)(2,1)}, u32[]{:S(2)}) copy-start(bf16[256,1,1024]{2,0,1:T(8,128)(2,1)} %get-tuple-element.136) | copy-start | bytes 1572868
  171.1 6.9 %copy-start.51 = (bf16[1024,2,1024]{2,1,0:T(2,128)(2,1)S(1)}, bf16[1024,2,1024]{2,1,0:T(2,128)(2,1)}, u32[]{:S(2)}) copy-start(bf16[1024,2,1024]{2,1,0:T(2,128)(2,1)} %param.23) | copy-start | bytes 12582916
  171.1 6.1 %collective-permute-start.6 = (f32[3,1024]{1,0:T(4,128)S(1)}, f32[3,1024]{1,0:T(4,128)S(1)}, u32[]{:S(2)}, u32[]{:S(2)}) collective-permute-start(f32[3,1024]{1,0:T(4,128)S(1)} %slice.234), channel_id=1, source_target_pairs={{2,0},{4,2},{6,4},{8,6},{10,8},{12,10},{14,12},{16,14},{18,16},{20... | collective-permute-start | bytes 36872 | tf_op jit(solution)/shard_map/ppermute | solution.py:23
  177.2 0.8 copy-start.13
  180.7 108.5 %reduce-scatter.2.cloned.1.call-start = ((), (), s32[]{:S(2)}) async-start(), calls=%async_computation.2 | async-start | bytes 1572864 | tf_op jit(solution)/shard_map/reduce_scatter | solution.py:344
  183.4 4.6 copy-start.4
  183.4 4.6 copy-start.12
  183.5 315.8 %all-reduce.8.cloned.1.call-start = ((), (), s32[]{:S(2)}) async-start(), calls=%async_computation.4 | async-start | bytes 26607616 | tf_op jit(solution)/shard_map/psum | solution.py:405
  188.0 2.8 copy-start.10
  188.1 2.8 copy-start.14
  188.1 2.8 copy-start.23
  188.1 2.8 copy-start.26
  195.6 0.7 copy-start.37
  195.6 0.7 copy-start.38
  195.7 29.2 %copy-start.33 = (f32[1024]{0:T(1024)S(1)}, f32[1024]{0:T(1024)}, u32[]{:S(2)}) copy-start(f32[1024]{0:T(1024)} %get-tuple-element.117) | copy-start | bytes 12292
  195.7 29.2 %copy-start.46 = (f32[1024]{0:T(1024)S(1)}, f32[1024]{0:T(1024)}, u32[]{:S(2)}) copy-start(f32[1024]{0:T(1024)} %get-tuple-element.113) | copy-start | bytes 12292
  195.7 92.6 %copy-start.45 = (f32[256]{0:T(256)S(1)}, f32[256]{0:T(256)}, u32[]{:S(2)}) copy-start(f32[256]{0:T(256)} %get-tuple-element.157) | copy-start | bytes 3076
  196.4 92.8 %copy-start.17 = (bf16[256,512]{1,0:T(8,128)(2,1)S(1)}, bf16[256,512]{1,0:T(8,128)(2,1)}, u32[]{:S(2)}) copy-start(bf16[256,512]{1,0:T(8,128)(2,1)} %param.21) | copy-start | bytes 786436
  499.3 15.5 %copy-start.21 = (f32[96,1024]{1,0:T(8,128)S(1)}, f32[96,1024]{1,0:T(8,128)}, u32[]{:S(2)}) copy-start(f32[96,1024]{1,0:T(8,128)} %get-tuple-element.170) | copy-start | bytes 1179652
  499.3 16.3 %copy-start.22 = (f32[64,1024]{1,0:T(8,128)S(1)}, f32[64,1024]{1,0:T(8,128)}, u32[]{:S(2)}) copy-start(f32[64,1024]{1,0:T(8,128)} %get-tuple-element.171) | copy-start | bytes 786436
  499.3 17.0 %copy-start.24 = (f32[16,1024]{1,0:T(8,128)S(1)}, f32[16,1024]{1,0:T(8,128)}, u32[]{:S(2)}) copy-start(f32[16,1024]{1,0:T(8,128)} %get-tuple-element.173) | copy-start | bytes 196612
  499.3 17.6 %copy-start.6 = (f32[1024,1024]{1,0:T(8,128)S(1)}, f32[1024,1024]{1,0:T(8,128)}, u32[]{:S(2)}) copy-start(f32[1024,1024]{1,0:T(8,128)} %get-tuple-element.175) | copy-start | bytes 12582916
  516.9 3.1 copy-start.1
Sparse Core Ops, SparseCore 0:
  41.7 22.6 all-gather.1
  180.8 42.4 all-reduce.5
  225.6 20.3 reduce-scatter.1
  251.9 247.3 all-reduce.7

commit v2 on v1

v2 whole, which is shorter than its diff:
```python
import functools

import jax
import jax.numpy as jnp
from jax import lax
from jax.experimental import pallas as pl
from jax.experimental.pallas import tpu as pltpu
from jax.sharding import PartitionSpec as P

epsilon = 1e-05
log2e = 1.4426950408889634
reset_step = 1e30
lanes = 128
halo = 16
body_rows = 32
scan_width = 512
vmem_bytes = 56 * 1024 * 1024
f32 = jnp.float32
bf16 = jnp.bfloat16
contract_first = (((0,), (0,)), ((), ()))
contract_last = (((1,), (1,)), ((), ()))


def passed_along(array, axis, by):
    peers = lax.axis_size(axis)
    pairs = [(i, i + by) for i in range(peers) if 0 <= i + by < peers]
    return lax.ppermute(array, axis, pairs)


def swapped(array, axis, bit):
    peers = lax.axis_size(axis)
    return lax.ppermute(array, axis, [(i, i ^ bit) for i in range(peers)])


def wide_bits():
    bit, bits = 1, []
    while bit < lax.axis_size("wide"):
        bits.append(bit)
        bit *= 2
    return bits


def summed_over_wide(keep, send):
    place = lax.axis_index("wide")
    bits = wide_bits()
    piece = keep + swapped(send.astype(bf16), "wide", bits[0]).astype(f32)
    for bit in bits[1:]:
        upper = (place & bit) != 0
        half = piece.shape[0] // 2
        low, high = piece[:half], piece[half:]
        away = jnp.where(upper, low, high).astype(bf16)
        piece = jnp.where(upper, high, low) + swapped(away, "wide", bit).astype(f32)
    held = piece.astype(bf16)
    for bit in reversed(bits):
        upper = (place & bit) != 0
        other = swapped(held, "wide", bit)
        held = jnp.concatenate([jnp.where(upper, other, held), jnp.where(upper, held, other)])
    return held


def halves_of(array, axis):
    upper = lax.axis_index("wide") & 1
    half = array.shape[axis] // 2
    return (
        lax.dynamic_slice_in_dim(array, upper * half, half, axis),
        lax.dynamic_slice_in_dim(array, (1 - upper) * half, half, axis),
    )


def weight_sum(left, right):
    mine, other = halves_of(left, 1)
    send = lax.dot_general(other, right, contract_first, preferred_element_type=f32)
    keep = lax.dot_general(mine, right, contract_first, preferred_element_type=f32)
    return summed_over_wide(keep, send)


def silu_slope(values):
    logistic = jax.nn.sigmoid(values)
    return logistic * (1.0 + values * (1.0 - logistic))


def softplus(values):
    return jnp.maximum(values, 0.0) + jnp.log1p(jnp.exp(-jnp.abs(values)))


def column_spec(rows, width=scan_width):
    return pl.BlockSpec((rows, width), lambda j: (0, j))


def part_spec(part, rows, width=scan_width):
    return pl.BlockSpec((None, rows, width), lambda j: (part, 0, j))


def whole_spec(rows, width):
    return pl.BlockSpec((rows, width), lambda j: (0, 0))


def call(kernel, name, width, in_specs, out_specs, out_shape, scratch, flops, *operands):
    moved = sum(a.size * a.dtype.itemsize for a in operands)
    return pl.pallas_call(
        kernel,
        grid=(width // scan_width,),
        in_specs=in_specs,
        out_specs=out_specs,
        out_shape=out_shape,
        scratch_shapes=scratch,
        compiler_params=pltpu.CompilerParams(vmem_limit_bytes=vmem_bytes),
        cost_estimate=pl.CostEstimate(flops=flops, bytes_accessed=moved, transcendentals=0),
        name=name,
    )(*operands)


def conv_kernel(
    inner_ref,
    conv_weight_ref,
    conv_bias_ref,
    select_ref,
    mask_ref,
    convolved_ref,
    act_ref,
    selected_ref,
    inner,
):
    rows = act_ref.shape[0]
    taps = conv_weight_ref.shape[0]
    inner[...] = inner_ref[...].astype(f32)
    total = conv_bias_ref[...] + conv_weight_ref[taps - 1 :, :] * inner[halo:, :]
    for lag in range(1, taps):
        earlier = inner[pl.ds(halo - lag, rows), :] * mask_ref[:, lag : lag + 1]
        total = total + conv_weight_ref[taps - 1 - lag : taps - lag, :] * earlier
    convolved_ref[...] = total
    act = (total * jax.nn.sigmoid(total)).astype(bf16)
    act_ref[...] = act
    part = lax.dot_general(select_ref[...], act, contract_last, preferred_element_type=f32)

    @pl.when(pl.program_id(0) == 0)
    def _():
        selected_ref[...] = part

    @pl.when(pl.program_id(0) > 0)
    def _():
        selected_ref[...] += part


def convolve(projected, conv_weight, conv_bias, select_weight, masks):
    parts, extended, width = projected.shape
    rows = extended - halo
    taps = conv_weight.shape[0]
    columns = select_weight.shape[0]
    return call(
        conv_kernel,
        "convolve",
        width,
        [
            part_spec(0, extended),
            column_spec(taps),
            column_spec(1),
            column_spec(columns),
            whole_spec(rows, masks.shape[1]),
        ],
        [column_spec(rows), column_spec(rows), whole_spec(columns, rows)],
        [
            jax.ShapeDtypeStruct((rows, width), f32),
            jax.ShapeDtypeStruct((rows, width), bf16),
            jax.ShapeDtypeStruct((columns, rows), f32),
        ],
        [pltpu.VMEM((extended, scan_width), f32)],
        4_000_000_000,
        projected,
        conv_weight,
        conv_bias,
        select_weight,
        masks,
    )


def coef_columns(coef, block):
    per_tile = lanes // body_rows
    start = pl.multiple_of((block // per_tile) * lanes, lanes)
    tile = coef[:, pl.ds(start, lanes)]
    back = body_rows * lax.rem(block, per_tile)
    return pltpu.roll(tile, lax.rem(lanes - back, lanes), 1)


def ends_kernel(
    selected_ref,
    other_ref,
    step_weight_ref,
    step_bias_ref,
    act_ref,
    gate_ref,
    gated_grad_ref,
    mask_ref,
    decay_log_ref,
    step_pre_ref,
    step_ref,
    ends_ref,
    coef,
    held_step,
    drive,
    scan_grad,
):
    rows = act_ref.shape[0]
    count = decay_log_ref.shape[0]
    rank = step_weight_ref.shape[0]
    decay2 = -jnp.exp(decay_log_ref[...]) * log2e
    selected = selected_ref[...] + other_ref[...]
    coef[...] = selected[rank:, :]
    step_low = selected[:rank, :].astype(bf16)
    step_pre = step_bias_ref[...] + lax.dot_general(
        step_low, step_weight_ref[...], contract_first, preferred_element_type=f32
    )
    step_pre_ref[...] = step_pre
    step = softplus(step_pre)
    step_ref[...] = step
    held_step[...] = jnp.where(mask_ref[:, 1:2] > 0.0, step, reset_step)
    drive[...] = step * act_ref[...].astype(f32)
    gate = gate_ref[...].astype(f32)
    scan_grad[...] = gated_grad_ref[...] * (gate * jax.nn.sigmoid(gate))
    zero = jnp.zeros(decay2.shape, f32)

    def body(block, carried):
        state, product, adjoint = carried
        columns = coef_columns(coef, block)
        for i in range(body_rows):
            row = pl.ds(block * body_rows + i, 1)
            factor = jnp.exp2(held_step[row, :] * decay2)
            state = factor * state + columns[:count, i : i + 1] * drive[row, :]
            product = factor * product
            adjoint = adjoint + product * (columns[count:, i : i + 1] * scan_grad[row, :])
        return state, product, adjoint

    state, product, adjoint = lax.fori_loop(0, rows // body_rows, body, (zero, zero + 1.0, zero))
    ends_ref[:count, :] = state
    ends_ref[count : 2 * count, :] = adjoint
    total = jnp.sum(held_step[...], axis=0, keepdims=True)
    ends_ref[2 * count :, :] = jnp.broadcast_to(total, (8, total.shape[1]))


def scan_ends(
    selected, other, step_weight, step_bias, act, projected, gated_grad, masks, decay_log
):
    rows, width = act.shape
    count = decay_log.shape[0]
    columns = selected.shape[0]
    rank = step_weight.shape[0]
    return call(
        ends_kernel,
        "scan_ends",
        width,
        [
            whole_spec(columns, rows),
            whole_spec(columns, rows),
            column_spec(rank),
            column_spec(1),
            column_spec(rows),
            pl.BlockSpec((None, rows, scan_width), lambda j: (0, 0, j)),
            column_spec(rows),
            whole_spec(rows, masks.shape[1]),
            column_spec(count),
        ],
        [column_spec(rows), column_spec(rows), column_spec(2 * count + 8)],
        [
            jax.ShapeDtypeStruct((rows, width), f32),
            jax.ShapeDtypeStruct((rows, width), f32),
            jax.ShapeDtypeStruct((2 * count + 8, width), f32),
        ],
        [pltpu.VMEM((2 * count, rows), f32)] + [pltpu.VMEM((rows, scan_width), f32)] * 3,
        10_000_000_000,
        selected,
        other,
        step_weight,
        step_bias,
        act,
        projected,
        gated_grad,
        masks,
        decay_log,
    )


def lane_tiles(values):
    return [values[:, k : k + lanes] for k in range(0, values.shape[1], lanes)]


def tree_sum(parts):
    while len(parts) > 1:
        odd = parts[len(parts) // 2 * 2 :]
        parts = [a + b for a, b in zip(parts[0::2], parts[1::2])] + odd
    return parts[0]


def keep_halves(scratch, i, values):
    for k, tile in enumerate(lane_tiles(values)):
        at = (k * body_rows + i) * 8
        scratch[at : at + 8, :] = tile[:8] + tile[8:]


def put_state_sums(scratch, out_ref, block):
    for group in range(body_rows // 8):
        row = pl.ds(pl.multiple_of(block * body_rows + group * 8, 8), 8)
        for k in range(out_ref.shape[1] // lanes):
            at = (k * body_rows + group * 8) * 8
            total = tree_sum([scratch[pl.ds(at + n, 8, stride=8), :] for n in range(8)])
            out_ref[row, k * lanes : (k + 1) * lanes] = total


def lane_sums(values):
    ones = jnp.ones((8, lanes), bf16)
    high = values.astype(bf16)
    low = (values - high.astype(f32)).astype(bf16)
    total = lax.dot_general(ones, high, contract_last, preferred_element_type=f32)
    total += lax.dot_general(ones, low, contract_last, preferred_element_type=f32)
    return total[:1, :]


def scan_kernel(
    selected_ref,
    other_ref,
    step_pre_ref,
    step_ref,
    act_ref,
    gate_ref,
    gated_grad_ref,
    mask_ref,
    decay_log_ref,
    entry_ref,
    tail_ref,
    skip_ref,
    step_weight_ref,
    gated_ref,
    gate_grad_ref,
    act_grad_ref,
    select_grad_ref,
    small_ref,
    coef,
    held_step,
    drive,
    scan_grad,
    scanned,
    weighted,
    states,
    factors,
    halves,
    more_halves,
    in_sum,
    read_sum,
):
    rows = step_ref.shape[0]
    count = decay_log_ref.shape[0]
    rank = step_weight_ref.shape[0]
    blocks = rows // body_rows
    first = pl.program_id(0) == 0
    last = pl.program_id(0) == pl.num_programs(0) - 1
    decay = -jnp.exp(decay_log_ref[...])
    decay2 = decay * log2e
    selected = selected_ref[...] + other_ref[...]
    coef[...] = selected[rank:, :]
    step_low = selected[:rank, :].astype(bf16)
    step = step_ref[...]
    act = act_ref[...].astype(f32)
    held_step[...] = jnp.where(mask_ref[:, 1:2] > 0.0, step, reset_step)
    drive[...] = step * act
    states[:count, :] = entry_ref[...]

    @pl.when(first)
    def _():
        in_sum[...] = jnp.zeros(in_sum.shape, f32)
        read_sum[...] = jnp.zeros(read_sum.shape, f32)
        select_grad_ref[...] = jnp.zeros(select_grad_ref.shape, f32)

    def at_token(t):
        return pl.ds(pl.multiple_of(t * count, count), count)

    def forward(block, state):
        columns = coef_columns(coef, block)
        for i in range(body_rows):
            t = block * body_rows + i
            row = pl.ds(t, 1)
            factor = jnp.exp2(held_step[row, :] * decay2)
            state = factor * state + columns[:count, i : i + 1] * drive[row, :]
            factors[at_token(t), :] = factor
            states[at_token(t + 1), :] = state
            keep_halves(halves, i, columns[count:, i : i + 1] * state)
        put_state_sums(halves, scanned, block)
        return state

    lax.fori_loop(0, blocks, forward, entry_ref[...])

    gate = gate_ref[...].astype(f32)
    logistic = jax.nn.sigmoid(gate)
    gate_act = gate * logistic
    gated_grad = gated_grad_ref[...]
    grads = gated_grad * gate_act
    scan_grad[...] = grads
    total = scanned[...] + skip_ref[...] * act
    gated_ref[...] = (total * gate_act).astype(bf16)
    slope = logistic * (1.0 + gate * (1.0 - logistic))
    gate_grad_ref[...] = (gated_grad * total * slope).astype(bf16)
    small_ref[rank + count : rank + count + 1, :] = jnp.sum(grads * act, axis=0, keepdims=True)

    def backward(k, carried):
        adjoint, decay_grad = carried
        block = blocks - 1 - k
        columns = coef_columns(coef, block)
        for i in range(body_rows - 1, -1, -1):
            t = block * body_rows + i
            row = pl.ds(t, 1)
            grad = scan_grad[row, :]
            summed = columns[count:, i : i + 1] * grad + adjoint
            read_sum[at_token(t), :] += tree_sum(lane_tiles(grad * states[at_token(t + 1), :]))
            in_sum[at_token(t), :] += tree_sum(lane_tiles(summed * drive[row, :]))
            keep_halves(halves, i, summed * columns[:count, i : i + 1])
            adjoint = factors[at_token(t), :] * summed
            held = adjoint * states[at_token(t), :]
            decay_grad = decay_grad + held * step_ref[row, :]
            keep_halves(more_halves, i, held * decay)
        put_state_sums(halves, weighted, block)
        put_state_sums(more_halves, scanned, block)
        return adjoint, decay_grad

    ignored, decay_grad = lax.fori_loop(
        0, blocks, backward, (tail_ref[...], jnp.zeros(decay.shape, f32))
    )
    act_grad_ref[...] = step * weighted[...] + skip_ref[...] * scan_grad[...]
    step_grad = act * weighted[...] + scanned[...]
    pre_grad = (step_grad * jax.nn.sigmoid(step_pre_ref[...])).astype(bf16)
    small_ref[:rank, :] = jnp.dot(step_low, pre_grad, preferred_element_type=f32)
    small_ref[rank : rank + count, :] = decay_grad * decay
    bias_grad = jnp.sum(pre_grad.astype(f32), axis=0, keepdims=True)
    small_ref[rank + count + 1 : rank + count + 2, :] = bias_grad
    spare = small_ref.shape[0] - (rank + count + 2)
    small_ref[rank + count + 2 :, :] = jnp.zeros((spare, small_ref.shape[1]), f32)
    select_grad_ref[:rank, :] += lax.dot_general(
        step_weight_ref[...], pre_grad, contract_last, preferred_element_type=f32
    )

    @pl.when(last)
    def _():
        for n in range(count):
            at = pl.ds(n, rows, stride=count)
            select_grad_ref[rank + n : rank + n + 1, :] = lane_sums(in_sum[at, :])
            select_grad_ref[rank + count + n : rank + count + n + 1, :] = lane_sums(read_sum[at, :])


def scan_full(
    selected,
    other,
    step_pre,
    step,
    act,
    projected,
    gated_grad,
    masks,
    decay_log,
    entry,
    tail,
    skip_gain,
    step_weight,
):
    rows, width = step.shape
    count = decay_log.shape[0]
    columns = selected.shape[0]
    rank = step_weight.shape[0]
    half_rows = 8 * body_rows * (scan_width // lanes)
    small = rank + count + 16
    return call(
        scan_kernel,
        "scan_full",
        width,
        [
            whole_spec(columns, rows),
            whole_spec(columns, rows),
            column_spec(rows),
            column_spec(rows),
            column_spec(rows),
            pl.BlockSpec((None, rows, scan_width), lambda j: (0, 0, j)),
            column_spec(rows),
            whole_spec(rows, masks.shape[1]),
            column_spec(count),
            column_spec(count),
            column_spec(count),
            column_spec(1),
            column_spec(rank),
        ],
        [column_spec(rows)] * 3 + [whole_spec(columns, rows), column_spec(small)],
        [
            jax.ShapeDtypeStruct((rows, width), bf16),
            jax.ShapeDtypeStruct((rows, width), bf16),
            jax.ShapeDtypeStruct((rows, width), f32),
            jax.ShapeDtypeStruct((columns, rows), f32),
            jax.ShapeDtypeStruct((small, width), f32),
        ],
        [pltpu.VMEM((2 * count, rows), f32)]
        + [pltpu.VMEM((rows, scan_width), f32)] * 5
        + [
            pltpu.VMEM(((rows + 1) * count, scan_width), f32),
            pltpu.VMEM((rows * count, scan_width), f32),
            pltpu.VMEM((half_rows, lanes), f32),
            pltpu.VMEM((half_rows, lanes), f32),
            pltpu.VMEM((rows * count, lanes), f32),
            pltpu.VMEM((rows * count, lanes), f32),
        ],
        24_000_000_000,
        selected,
        other,
        step_pre,
        step,
        act,
        projected,
        gated_grad,
        masks,
        decay_log,
        entry,
        tail,
        skip_gain,
        step_weight,
    )


def conv_grad_kernel(
    select_grad_ref,
    other_ref,
    select_ref,
    act_grad_ref,
    convolved_ref,
    act_ref,
    inner_ref,
    conv_weight_ref,
    mask_ref,
    inner_grad_ref,
    edge_ref,
    small_ref,
    inner,
    shifted,
):
    rows = act_ref.shape[0]
    taps = conv_weight_ref.shape[0]
    columns = select_ref.shape[0]
    select_grad = (select_grad_ref[...] + other_ref[...]).astype(bf16)
    total = act_grad_ref[...] + lax.dot_general(
        select_grad, select_ref[...], contract_first, preferred_element_type=f32
    )
    conv_grad = total * silu_slope(convolved_ref[...])
    small_ref[:columns, :] = jnp.dot(select_grad, act_ref[...], preferred_element_type=f32)
    inner[...] = inner_ref[...].astype(f32)
    edges = jnp.zeros((8, conv_grad.shape[1]), f32)
    shifted[:8, :] = edges
    shifted[rows + 8 :, :] = edges
    out = conv_weight_ref[taps - 1 :, :] * conv_grad
    before = edges
    small_ref[columns + taps - 1 : columns + taps, :] = jnp.sum(
        conv_grad * inner[halo:, :], axis=0, keepdims=True
    )
    for lag in range(1, taps):
        masked = conv_grad * mask_ref[:, lag : lag + 1]
        at = taps - 1 - lag
        small_ref[columns + at : columns + at + 1, :] = jnp.sum(
            masked * inner[pl.ds(halo - lag, rows), :], axis=0, keepdims=True
        )
        shifted[8 : rows + 8, :] = masked
        weight = conv_weight_ref[at : at + 1, :]
        out = out + weight * shifted[pl.ds(8 + lag, rows), :]
        before = before + weight * shifted[pl.ds(lag, 8), :]
    small_ref[columns + taps : columns + taps + 1, :] = jnp.sum(conv_grad, axis=0, keepdims=True)
    spare = small_ref.shape[0] - (columns + taps + 1)
    small_ref[columns + taps + 1 :, :] = jnp.zeros((spare, small_ref.shape[1]), f32)
    inner_grad_ref[...] = out.astype(bf16)
    edge_ref[:8, :] = before
    edge_ref[8:, :] = out[rows - 8 :, :]


def convolve_grad(
    select_grad, other, select_weight, act_grad, convolved, act, projected, conv_weight, masks
):
    rows, width = act.shape
    extended = rows + halo
    columns = select_weight.shape[0]
    taps = conv_weight.shape[0]
    small = columns + 16
    return call(
        conv_grad_kernel,
        "convolve_grad",
        width,
        [
            whole_spec(columns, rows),
            whole_spec(columns, rows),
            column_spec(columns),
            column_spec(rows),
            column_spec(rows),
            column_spec(rows),
            part_spec(0, extended),
            column_spec(taps),
            whole_spec(rows, masks.shape[1]),
        ],
        [column_spec(rows), column_spec(16), column_spec(small)],
        [
            jax.ShapeDtypeStruct((rows, width), bf16),
            jax.ShapeDtypeStruct((16, width), f32),
            jax.ShapeDtypeStruct((small, width), f32),
        ],
        [pltpu.VMEM((extended, scan_width), f32), pltpu.VMEM((rows + 16, scan_width), f32)],
        6_000_000_000,
        select_grad,
        other,
        select_weight,
        act_grad,
        convolved,
        act,
        projected,
        conv_weight,
        masks,
    )


def join_kernel(inner_ref, gate_ref, out_ref):
    out_ref[:, 0, :] = inner_ref[...].astype(f32)
    out_ref[:, 1, :] = gate_ref[...].astype(f32)


def joined(inner, gate):
    depth, width = inner.shape
    rows = 256
    spec = pl.BlockSpec((rows, width), lambda j: (j, 0))
    return pl.pallas_call(
        join_kernel,
        grid=(depth // rows,),
        in_specs=[spec, spec],
        out_specs=pl.BlockSpec((rows, 2, width), lambda j: (j, 0, 0)),
        out_shape=jax.ShapeDtypeStruct((depth, 2, width), f32),
        compiler_params=pltpu.CompilerParams(vmem_limit_bytes=vmem_bytes),
        name="joined",
    )(inner, gate)


def carried(ends, decay):
    count = decay.shape[0]
    place = lax.axis_index("wide")

    def split(packed):
        return packed[:count], packed[count : 2 * count], packed[2 * count : 2 * count + 1]

    def through(total):
        return jnp.exp(decay * total)

    zero = jnp.zeros(decay.shape, f32)
    none = jnp.zeros((1, decay.shape[1]), f32)
    before, before_steps, after, after_steps = zero, none, zero, none
    packed = ends
    for bit in (1, 2):
        second = (place & bit) != 0
        own = split(packed)
        other = split(swapped(packed, "wide", bit))
        early = [jnp.where(second, b, a) for a, b in zip(own, other)]
        late = [jnp.where(second, a, b) for a, b in zip(own, other)]
        before = before + jnp.where(second, through(before_steps) * other[0], 0.0)
        before_steps = before_steps + jnp.where(second, other[2], 0.0)
        after = after + jnp.where(second, 0.0, through(after_steps) * other[1])
        after_steps = after_steps + jnp.where(second, 0.0, other[2])
        state = late[0] + through(late[2]) * early[0]
        adjoint = early[1] + through(early[2]) * late[1]
        packed = jnp.concatenate(
            [state, adjoint, jnp.broadcast_to(early[2] + late[2], (8, decay.shape[1]))]
        )
    from_before = passed_along(packed[:count], "wide", 4)
    from_after = passed_along(packed[count : 2 * count], "wide", -4)
    return (
        before + through(before_steps) * from_before,
        after + through(after_steps) * from_after,
    )


def local(
    tokens,
    norm_gain,
    in_weight,
    conv_weight,
    conv_bias,
    select_weight,
    step_weight,
    step_bias,
    decay_log,
    skip_gain,
    out_weight,
    segment_ids,
    cotangent,
):
    rows, features = tokens.shape
    taps = conv_weight.shape[0]
    columns = select_weight.shape[0]
    rank = step_weight.shape[0]
    count = decay_log.shape[0]
    right_half = lax.axis_index("narrow") == 1

    def both_halves(own, other):
        return jnp.concatenate(
            [jnp.where(right_half, other, own), jnp.where(right_half, own, other)], axis=1
        )

    last_ids = segment_ids[rows - halo :]
    same_as_last = (last_ids == segment_ids[rows - 1 :])[:, None]
    edge_rows = jnp.where(same_as_last, tokens[rows - halo :], jnp.zeros((), tokens.dtype))
    before_own = passed_along(edge_rows, "wide", 1)
    sent = jnp.concatenate([before_own, tokens])
    whole_ext = both_halves(sent, swapped(sent, "narrow", 1)).astype(f32)
    cot_whole = both_halves(cotangent, swapped(cotangent, "narrow", 1))

    padded_ids = jnp.concatenate([jnp.broadcast_to(segment_ids[:1], (taps - 1,)), segment_ids])
    masks = jnp.stack(
        [
            (padded_ids[taps - 1 - lag : taps - 1 - lag + rows] == segment_ids).astype(f32)
            for lag in range(taps)
        ]
        + [jnp.zeros((rows,), f32)] * (8 - taps),
        axis=1,
    )

    inverse_ext = lax.rsqrt(jnp.mean(whole_ext * whole_ext, axis=1, keepdims=True) + epsilon)
    normed_ext = (whole_ext * inverse_ext * norm_gain).astype(bf16)
    projected = jnp.einsum(
        "td,dce->cte", normed_ext, in_weight, preferred_element_type=f32
    ).astype(bf16)
    gate_half = projected[1:, halo:]
    convolved, act, selected = convolve(
        projected, conv_weight, conv_bias[None], select_weight, masks
    )
    other_selected = swapped(selected, "narrow", 1)
    gated_grad = lax.dot_general(
        cot_whole, out_weight, contract_last, preferred_element_type=f32
    )
    step_pre, step, ends = scan_ends(
        selected,
        other_selected,
        step_weight,
        step_bias[None],
        act,
        gate_half,
        gated_grad,
        masks,
        decay_log,
    )
    entry, tail = carried(ends, -jnp.exp(decay_log))
    gated, gate_grad, act_grad, select_grad, scan_small = scan_full(
        selected,
        other_selected,
        step_pre,
        step,
        act,
        gate_half,
        gated_grad,
        masks,
        decay_log,
        entry,
        tail,
        skip_gain[None],
        step_weight,
    )
    other_select_grad = swapped(select_grad, "narrow", 1)
    out_weight_grad = weight_sum(gated, cot_whole)
    normed = normed_ext[halo:]
    gate_weight_grad = weight_sum(normed, gate_grad)

    def narrow_halves(array):
        low, high = array[:, :features], array[:, features:]
        return jnp.where(right_half, high, low), jnp.where(right_half, low, high)

    out_part = jnp.dot(gated, out_weight, preferred_element_type=f32)
    out_mine, out_other = narrow_halves(out_part)
    out_sum = out_mine + swapped(out_other, "narrow", 1)
    layer_out = (tokens.astype(f32) + out_sum).astype(bf16)

    inner_main, edges, conv_small = convolve_grad(
        select_grad,
        other_select_grad,
        select_weight,
        act_grad,
        convolved,
        act,
        projected,
        conv_weight,
        masks,
    )
    from_next = passed_along(edges[:8], "wide", -1)
    last_rows = edges[8:] + jnp.where(same_as_last[halo - 8 :], from_next, 0.0)
    inner_grad = jnp.concatenate([inner_main[: rows - 8], last_rows.astype(bf16)])
    normed_part = jnp.einsum(
        "cte,dce->td", jnp.stack([inner_grad, gate_grad]), in_weight, preferred_element_type=f32
    )
    inner_weight_grad = weight_sum(normed, inner_grad)

    whole = whole_ext[halo:]
    inverse = inverse_ext[halo:]
    gain_part = jnp.sum(normed_part * whole * inverse, axis=0, keepdims=True)
    row_part = jnp.sum(normed_part * norm_gain * whole, axis=1, keepdims=True)
    normed_mine, normed_other = narrow_halves(normed_part)
    row_sum = row_part + swapped(row_part, "narrow", 1)
    normed_sum = normed_mine + swapped(normed_other, "narrow", 1)
    gain_mine = jnp.where(right_half, norm_gain[features:], norm_gain[:features])
    whole_grad = inverse * (gain_mine * normed_sum) - tokens.astype(f32) * (
        inverse * inverse * inverse
    ) * (row_sum / (2 * features))
    tokens_grad = (whole_grad + cotangent.astype(f32)).astype(bf16)

    gain_sum = gain_part + swapped(gain_part, "narrow", 1)
    spare = -(scan_small.shape[0] + conv_small.shape[0] + 1) % 256
    small = jnp.concatenate(
        [scan_small, conv_small, gain_sum, jnp.zeros((spare, gain_sum.shape[1]), f32)]
    )
    small_sum = summed_over_wide(*halves_of(small, 0)).astype(f32)
    scan_sum = small_sum[: scan_small.shape[0]]
    conv_sum = small_sum[scan_small.shape[0] : scan_small.shape[0] + conv_small.shape[0]]
    norm_gain_grad = small_sum[scan_small.shape[0] + conv_small.shape[0]]
    return (
        layer_out,
        tokens_grad,
        norm_gain_grad,
        joined(inner_weight_grad, gate_weight_grad),
        conv_sum[columns : columns + taps],
        conv_sum[columns + taps],
        conv_sum[:columns],
        scan_sum[:rank],
        scan_sum[rank + count + 1],
        scan_sum[rank : rank + count],
        scan_sum[rank + count],
        out_weight_grad.astype(f32),
    )


def solution(mesh):
    placed = (
        P("wide", "narrow"),
        P(),
        P(None, None, "narrow"),
        P(None, "narrow"),
        P("narrow"),
        P(None, "narrow"),
        P(None, "narrow"),
        P("narrow"),
        P(None, "narrow"),
        P("narrow"),
        P("narrow", None),
        P("wide"),
        P("wide", "narrow"),
    )
    return jax.shard_map(
        local,
        mesh=mesh,
        in_specs=placed,
        out_specs=(
            P("wide", "narrow"),
            P("wide", "narrow"),
            P(),
            P(None, None, "narrow"),
            P(None, "narrow"),
            P("narrow"),
            P(None, "narrow"),
            P(None, "narrow"),
            P("narrow"),
            P(None, "narrow"),
            P("narrow"),
            P("narrow", None),
        ),
        check_vma=False,
    )
```

time: 528 us -> 302 us (0.57)
  waiting for transfers between devices: 254 us -> 141 us
  blocking collectives: 101 us -> 0 us
  starting transfers between devices: 14.4 us -> 58 us
  local copies, waits for them, and re-layouts: 39.8 us -> 10.1 us
  matrix products: 33.2 us -> 12.1 us
  Pallas kernels: 33.6 us -> 52.7 us
  between operations: 14.4 us -> 1.46 us
  other arithmetic: 35.2 us -> 25.8 us
    psum x2 -> x0, waiting for transfers between devices: 235 us -> none  [the longest x1 208 us: local(): lax.psum((in_weight_grad, out_weight_grad, conv_weight_grad, conv_bias_gr...]
    ppermute x2 -> x42, waiting for transfers between devices: 6.83 us -> 138 us  [swapped(): return lax.ppermute(array, axis, [(i, i ^ bit) for i in range(peers)])]
    psum x2 -> x0, blocking collectives: 72.8 us -> none  [the longest x1 63.4 us: local(): lax.psum((in_weight_grad, out_weight_grad, conv_weight_grad, conv_bias_gr...]
    ppermute x2 -> x42, starting transfers between devices: 1.47 us -> 48.4 us  [swapped(): return lax.ppermute(array, axis, [(i, i ^ bit) for i in range(peers)])]
    all_gather x3 -> x0, blocking collectives: 28.7 us -> none  [the longest x1 10.4 us: local(): lax.all_gather(select_weight, 'narrow', axis=1, tiled=True)]
    unnamed x111 -> x31, local copies, waits for them, and re-layouts: 23.7 us -> 1.36 us
    pallas_call x2 -> x5, Pallas kernels: 33.6 us -> 52.7 us  [the longest x4 46.3 us: call(): pl.pallas_call(kernel, grid=(width // scan_width,), in_specs=in_specs, ou...]
    dot_general x11 -> x9, matrix products: 29 us -> 10.4 us  [the longest x1 4.94 us: local(): jnp.einsum('td,dce->cte', normed_ext, in_weight, preferred_element_type=f32)]
  transfers between devices with their start and end apart: 11 -> 46, of which waited for: 7 -> 32; matrix products, arithmetic and copies ran while one was open for 6% -> 8% of each run, Pallas kernels for 0% -> 0%
where the time goes in v2:
time: 302 us; the launch traced here: 301 us
  waiting for transfers between devices  141 us (47%)
  starting transfers between devices  58 us (19%)
  Pallas kernels  52.7 us (17%)
  other arithmetic  25.8 us (9%)
  matrix products  12.1 us (4%)
  local copies, waits for them, and re-layouts  10.1 us (3%)
    ppermute x42, waiting for transfers between devices, swapped(): return lax.ppermute(array, axis, [(i, i ^ bit) for i in range(peers)])  138 us
    ppermute x42, starting transfers between devices, swapped(): return lax.ppermute(array, axis, [(i, i ^ bit) for i in range(peers)])  48.4 us
    pallas_call x4, Pallas kernels, call(): pl.pallas_call(kernel, grid=(width // scan_width,), in_specs=in_specs, ou...  46.3 us
    ppermute x4, starting transfers between devices, passed_along(): return lax.ppermute(array, axis, pairs)  9.65 us
    pallas_call x1, Pallas kernels, joined(): pl.pallas_call(join_kernel, grid=(depth // rows,), in_specs=[spec, spec],...  6.42 us
  transfers between devices with their start and end apart: 46, of which 32 were waited for; matrix products, arithmetic and copies ran while one was open for 8% of the time, Pallas kernels for 0%

profile of v2, /device:TPU:0, one launch (start us, length us, event | category | flops | bytes accessed | tf_op | source)
XLA Modules:
  0.0 300.7 jit_solution(17005346663069018329)
XLA Ops:
  0.7 1.4 fusion.48
  2.1 1.4 slice_compare_fusion
  4.3 2.3 collective-permute-start
  6.6 2.4 collective-permute-start.3
  10.9 1.5 compare_convert_fusion
  13.2 2.1 collective-permute-done.3
  16.3 4.9 %collective-permute-done.1 = bf16[272,512]{1,0:T(8,128)(2,1)} collective-permute-done((bf16[272,512]{1,0:T(8,128)(2,1)S(1)}, bf16[272,512]{1,0:T(8,128)(2,1)}, u32[]{:S(2)}, u32[]{:S(2)}) %collective-permute-start.1) | collective-permute-done | bytes 278560 | tf_op jit(solution)/shard_map/ppermute | solution.py:32
  22.6 4.9 %fusion.7.inner_ref = bf16[2,272,1024]{2,1,0:T(8,128)(2,1)} fusion(bf16[1024,2,1024]{2,1,0:T(2,128)(2,1)} %param.15, bf16[272,1024]{1,0:T(8,128)(2,1)S(1)} %multiply_convert_fusion), kind=kOutput, calls=%fused_computation.14 | convolution fusion | flops 1141407744 | bytes 5865472 | tf_op jit(solution)/shard_map/td,dce->cte/dot_general | solution.py:720
  27.5 3.5 %convolve.1 = (f32[256,1024]{1,0:T(8,128)}, bf16[256,1024]{1,0:T(8,128)(2,1)}, f32[96,256]{1,0:T(8,128)}) custom-call(bf16[2,272,1024]{2,1,0:T(8,128)(2,1)} %fusion.7.inner_ref, f32[4,1024]{1,0:T(4,128)} %conv_weight_ref.3, f32[1,1024]{1,0:T(1,128)} %bitcast.65, bf16[96,1024]{1,0:T(8,128)(2,1)} %select_ref.3, f32[256,8]{1,0:T(8,128)} %copy.33.mask_ref), custom_call_target="tpu_custom_call" | custom-call | flops 4000000000 | bytes 1339392 | tf_op jit(solution)/shard_map/convolve/pallas_call | solution.py:100
  31.0 2.6 collective-permute-start.2
  33.7 1.7 fusion.32.gated_grad_ref
  35.4 1.9 slice.263.gate_ref
  38.1 10.8 %scan_ends.1 = (f32[256,1024]{1,0:T(8,128)}, f32[256,1024]{1,0:T(8,128)}, f32[40,1024]{1,0:T(8,128)}) custom-call(f32[96,256]{1,0:T(8,128)} %get-tuple-element.26.selected_ref, f32[96,256]{1,0:T(8,128)} %copy-done.13, bf16[64,1024]{1,0:T(8,128)(2,1)} %step_weight_ref.3, f32[1,1024]{1,0:T(1,128)} %bitcast.66, bf16[256,1024]{1,0:T(8,128)(2,1)} %get-tuple-element.27.act_ref, ...), custom_call_target="tpu_custom_call" | custom-call | flops 10000000000 | bytes 2502656 | tf_op jit(solution)/shard_map/scan_ends/pallas_call | solution.py:100
  49.0 1.5 collective-permute-done.4
  52.9 1.9 collective-permute-start.5
  54.8 4.8 %collective-permute-done.5 = f32[40,1024]{1,0:T(8,128)} collective-permute-done((f32[40,1024]{1,0:T(8,128)}, f32[40,1024]{1,0:T(8,128)}, u32[]{:S(2)}, u32[]{:S(2)}) %collective-permute-start.5) | collective-permute-done | bytes 163872 | tf_op jit(solution)/shard_map/ppermute | solution.py:32
  62.6 4.5 %collective-permute-start.6 = (f32[16,1024]{1,0:T(8,128)S(1)}, f32[16,1024]{1,0:T(8,128)S(1)}, u32[]{:S(2)}, u32[]{:S(2)}) collective-permute-start(f32[16,1024]{1,0:T(8,128)S(1)} %get-tuple-element.94), channel_id=1, source_target_pairs={{0,8},{2,10},{4,12},{6,14},{8,16},{10,18},{12,20},{14,22},{16,24},... | collective-permute-start | bytes 196616 | tf_op jit(solution)/shard_map/ppermute | solution.py:27
  67.5 1.6 collective-permute-done.6
  69.1 1.6 multiply_add_fusion
  70.7 27.2 %scan_full.1 = (bf16[256,1024]{1,0:T(8,128)(2,1)}, bf16[256,1024]{1,0:T(8,128)(2,1)}, f32[256,1024]{1,0:T(8,128)}, f32[96,256]{1,0:T(8,128)}, f32[96,1024]{1,0:T(8,128)}) custom-call(f32[96,256]{1,0:T(8,128)} %get-tuple-element.26.selected_ref, f32[96,256]{1,0:T(8,128)} %copy-done.13, f32[256,1024]{1,0:T(8,128)} %get-tuple-element.28.step_pre_ref, ...), custom_call_target="tpu_custom_call" | custom-call | flops 24000000000 | bytes 4730880 | tf_op jit(solution)/shard_map/scan_full/pallas_call | solution.py:100
  97.9 1.7 collective-permute-start.9
  99.7 3.1 %collective-permute-done.9.other_ref = f32[96,256]{1,0:T(8,128)S(1)} collective-permute-done((f32[96,256]{1,0:T(8,128)}, f32[96,256]{1,0:T(8,128)S(1)}, u32[]{:S(2)}, u32[]{:S(2)}) %collective-permute-start.9) | collective-permute-done | bytes 98336 | tf_op jit(solution)/shard_map/ppermute | solution.py:32
  103.5 4.8 %convolve_grad.1 = (bf16[256,1024]{1,0:T(8,128)(2,1)}, f32[16,1024]{1,0:T(8,128)}, f32[112,1024]{1,0:T(8,128)}) custom-call(f32[96,256]{1,0:T(8,128)} %get-tuple-element.32.select_grad_ref, f32[96,256]{1,0:T(8,128)} %copy-done.14, bf16[96,1024]{1,0:T(8,128)(2,1)} %select_ref.3, f32[256,1024]{1,0:T(8,128)} %get-tuple-element.33.act_grad_ref, ...), custom_call_target="tpu_custom_call" | custom-call | flops 6000000000 | bytes 4153344 | tf_op jit(solution)/shard_map/convolve_grad/pallas_call | solution.py:100
  109.1 1.5 collective-permute-start.10
  112.3 1.9 multiply_reduce_fusion.1
  114.2 1.7 collective-permute-start.13
  115.9 2.0 collective-permute-done.13
  120.1 1.6 collective-permute-start.8
  121.8 2.2 collective-permute-start.15
  124.5 2.9 collective-permute-done.15
  127.5 2.0 collective-permute-start.16
  131.8 3.1 %collective-permute-start.17 = (bf16[16,1024]{1,0:T(8,128)(2,1)S(1)}, bf16[16,1024]{1,0:T(8,128)(2,1)S(1)}, u32[]{:S(2)}, u32[]{:S(2)}) collective-permute-start(bf16[16,1024]{1,0:T(8,128)(2,1)S(1)} %select_convert_fusion.11), channel_id=1, source_target_pairs={{0,16},{2,18},{4,20},{6,22},{8,24},{10,26},{12,28},{14,30},{16,0},... | collective-permute-start | bytes 98312 | tf_op jit(solution)/shard_map/ppermute | solution.py:32
  135.0 1.8 collective-permute-done.17
  136.9 3.0 %collective-permute-start.18 = (bf16[16,1024]{1,0:T(8,128)(2,1)S(1)}, bf16[16,1024]{1,0:T(8,128)(2,1)S(1)}, u32[]{:S(2)}, u32[]{:S(2)}) collective-permute-start(bf16[16,1024]{1,0:T(8,128)(2,1)S(1)} %add_convert_fusion.3), channel_id=1, source_target_pairs={{0,16},{2,18},{4,20},{6,22},{8,24},{10,26},{12,28},{14,30},{16,0},... | collective-permute-start | bytes 98312 | tf_op jit(solution)/shard_map/ppermute | solution.py:32
  142.6 8.7 %collective-permute-done.12 = f32[256,1]{0,1:T(1,128)S(1)} collective-permute-done((f32[256,1]{0,1:T(1,128)S(1)}, f32[256,1]{0,1:T(1,128)S(1)}, u32[]{:S(2)}, u32[]{:S(2)}) %collective-permute-start.12) | collective-permute-done | bytes 1056 | tf_op jit(solution)/shard_map/ppermute | solution.py:32
  152.4 3.1 %collective-permute-done.19 = bf16[32,1024]{1,0:T(8,128)(2,1)S(1)} collective-permute-done((bf16[32,1024]{1,0:T(8,128)(2,1)S(1)}, bf16[32,1024]{1,0:T(8,128)(2,1)S(1)}, u32[]{:S(2)}, u32[]{:S(2)}) %collective-permute-start.19) | collective-permute-done | bytes 65568 | tf_op jit(solution)/shard_map/ppermute | solution.py:32
  155.6 1.6 collective-permute-start.20
  158.3 3.4 %collective-permute-done.20 = bf16[64,1024]{1,0:T(8,128)(2,1)S(1)} collective-permute-done((bf16[64,1024]{1,0:T(8,128)(2,1)S(1)}, bf16[64,1024]{1,0:T(8,128)(2,1)S(1)}, u32[]{:S(2)}, u32[]{:S(2)}) %collective-permute-start.20) | collective-permute-done | bytes 131104 | tf_op jit(solution)/shard_map/ppermute | solution.py:32
  162.4 1.6 collective-permute-start.31
  166.0 1.6 collective-permute-start.23
  167.5 9.6 %collective-permute-done.31 = bf16[256,1024]{1,0:T(8,128)(2,1)S(1)} collective-permute-done((bf16[256,1024]{1,0:T(8,128)(2,1)S(1)}, bf16[256,1024]{1,0:T(8,128)(2,1)S(1)}, u32[]{:S(2)}, u32[]{:S(2)}) %collective-permute-start.31) | collective-permute-done | bytes 524320 | tf_op jit(solution)/shard_map/ppermute | solution.py:32
  177.5 1.6 collective-permute-start.32
  179.1 9.3 %collective-permute-done.39 = bf16[256,1024]{1,0:T(8,128)(2,1)S(1)} collective-permute-done((bf16[256,1024]{1,0:T(8,128)(2,1)S(1)}, bf16[256,1024]{1,0:T(8,128)(2,1)S(1)}, u32[]{:S(2)}, u32[]{:S(2)}) %collective-permute-start.39) | collective-permute-done | bytes 524320 | tf_op jit(solution)/shard_map/ppermute | solution.py:32
  188.7 1.6 collective-permute-start.40
  190.3 8.9 %collective-permute-done.23 = bf16[256,1024]{1,0:T(8,128)(2,1)S(1)} collective-permute-done((bf16[256,1024]{1,0:T(8,128)(2,1)S(1)}, bf16[256,1024]{1,0:T(8,128)(2,1)S(1)}, u32[]{:S(2)}, u32[]{:S(2)}) %collective-permute-start.23) | collective-permute-done | bytes 524320 | tf_op jit(solution)/shard_map/ppermute | solution.py:32
  199.5 1.6 collective-permute-start.24
  201.8 2.7 collective-permute-start.41
  204.5 6.1 %collective-permute-done.24 = bf16[128,1024]{1,0:T(8,128)(2,1)S(1)} collective-permute-done((bf16[128,1024]{1,0:T(8,128)(2,1)S(1)}, bf16[128,1024]{1,0:T(8,128)(2,1)S(1)}, u32[]{:S(2)}, u32[]{:S(2)}) %collective-permute-start.24) | collective-permute-done | bytes 262176 | tf_op jit(solution)/shard_map/ppermute | solution.py:32
  210.7 2.0 collective-permute-start.25
  212.7 1.6 collective-permute-done.33
  214.4 11.1 %collective-permute-done.41 = bf16[64,1024]{1,0:T(8,128)(2,1)S(1)} collective-permute-done((bf16[64,1024]{1,0:T(8,128)(2,1)S(1)}, bf16[64,1024]{1,0:T(8,128)(2,1)S(1)}, u32[]{:S(2)}, u32[]{:S(2)}) %collective-permute-start.41) | collective-permute-done | bytes 131104 | tf_op jit(solution)/shard_map/ppermute | solution.py:32
  225.7 5.5 %collective-permute-done.25 = bf16[64,1024]{1,0:T(8,128)(2,1)S(1)} collective-permute-done((bf16[64,1024]{1,0:T(8,128)(2,1)S(1)}, bf16[64,1024]{1,0:T(8,128)(2,1)S(1)}, u32[]{:S(2)}, u32[]{:S(2)}) %collective-permute-start.25) | collective-permute-done | bytes 131104 | tf_op jit(solution)/shard_map/ppermute | solution.py:32
  231.3 2.7 collective-permute-done.34
  234.1 2.6 collective-permute-done.42
  239.0 10.4 %collective-permute-done.43 = bf16[128,1024]{1,0:T(8,128)(2,1)S(1)} collective-permute-done((bf16[128,1024]{1,0:T(8,128)(2,1)S(1)}, bf16[128,1024]{1,0:T(8,128)(2,1)S(1)}, u32[]{:S(2)}, u32[]{:S(2)}) %collective-permute-start.43) | collective-permute-done | bytes 262176 | tf_op jit(solution)/shard_map/ppermute | solution.py:32
  249.5 1.8 collective-permute-start.44
  251.9 3.0 %collective-permute-done.27 = bf16[128,1024]{1,0:T(8,128)(2,1)S(1)} collective-permute-done((bf16[128,1024]{1,0:T(8,128)(2,1)S(1)}, bf16[128,1024]{1,0:T(8,128)(2,1)S(1)}, u32[]{:S(2)}, u32[]{:S(2)}) %collective-permute-start.27) | collective-permute-done | bytes 262176 | tf_op jit(solution)/shard_map/ppermute | solution.py:32
  255.1 1.8 collective-permute-start.28
  256.9 7.5 %collective-permute-done.44 = bf16[256,1024]{1,0:T(8,128)(2,1)S(1)} collective-permute-done((bf16[256,1024]{1,0:T(8,128)(2,1)S(1)}, bf16[256,1024]{1,0:T(8,128)(2,1)S(1)}, u32[]{:S(2)}, u32[]{:S(2)}) %collective-permute-start.44) | collective-permute-done | bytes 524320 | tf_op jit(solution)/shard_map/ppermute | solution.py:32
  266.9 8.7 %collective-permute-done.36 = bf16[256,1024]{1,0:T(8,128)(2,1)S(1)} collective-permute-done((bf16[256,1024]{1,0:T(8,128)(2,1)S(1)}, bf16[256,1024]{1,0:T(8,128)(2,1)S(1)}, u32[]{:S(2)}, u32[]{:S(2)}) %collective-permute-start.36) | collective-permute-done | bytes 524320 | tf_op jit(solution)/shard_map/ppermute | solution.py:32
  276.0 9.8 %collective-permute-done.28 = bf16[256,1024]{1,0:T(8,128)(2,1)S(1)} collective-permute-done((bf16[256,1024]{1,0:T(8,128)(2,1)S(1)}, bf16[256,1024]{1,0:T(8,128)(2,1)S(1)}, u32[]{:S(2)}, u32[]{:S(2)}) %collective-permute-start.28) | collective-permute-done | bytes 524320 | tf_op jit(solution)/shard_map/ppermute | solution.py:32
  288.3 2.4 maximum_convert_fusion
  291.9 2.4 pad_maximum_fusion
  294.3 6.4 %joined.1 = f32[1024,2,1024]{2,1,0:T(2,128)} custom-call(bf16[1024,1024]{1,0:T(8,128)(2,1)} %get-tuple-element.109.inner_ref, bf16[1024,1024]{1,0:T(8,128)(2,1)} %get-tuple-element.110.gate_ref), custom_call_target="tpu_custom_call" | custom-call | tf_op jit(solution)/shard_map/joined/pallas_call | solution.py:625
  (176 shorter events, 40.3 us)
Async XLA Ops:
  0.6 33.0 %copy-start = (bf16[1024,1024]{1,0:T(8,128)(2,1)S(1)}, bf16[1024,1024]{1,0:T(8,128)(2,1)}, u32[]{:S(2)}) copy-start(bf16[1024,1024]{1,0:T(8,128)(2,1)} %param.23) | copy-start | bytes 6291460
  0.7 21.7 %copy-start.11 = (f32[1024]{0:T(1024)S(1)}, f32[1024]{0:T(1024)}, u32[]{:S(2)}) copy-start(f32[1024]{0:T(1024)} %param.14) | copy-start | bytes 12292
  4.3 4.8 %collective-permute-start = (bf16[16,512]{1,0:T(8,128)(2,1)S(1)}, bf16[16,512]{1,0:T(8,128)(2,1)S(1)}, u32[]{:S(2)}, u32[]{:S(2)}) collective-permute-start(bf16[16,512]{1,0:T(8,128)(2,1)S(1)} %slice_select_fusion.2), channel_id=1, source_target_pairs={{0,2},{2,4},{4,6},{6,8},{8,10},{10,12},{12,14},{14,16},{16,18},{18... | collective-permute-start | bytes 49160 | tf_op jit(solution)/shard_map/ppermute | solution.py:27
  6.6 8.7 %collective-permute-start.3 = (bf16[256,512]{1,0:T(8,128)(2,1)}, bf16[256,512]{1,0:T(8,128)(2,1)S(1)}, u32[]{:S(2)}, u32[]{:S(2)}) collective-permute-start(bf16[256,512]{1,0:T(8,128)(2,1)} %param.25), channel_id=1, source_target_pairs={{0,1},{1,0},{2,3},{3,2},{4,5},{5,4},{6,7},{7,6},{8,9},{9,8},{10,11... | collective-permute-start | bytes 786440 | tf_op jit(solution)/shard_map/ppermute | solution.py:32
  10.0 11.1 %collective-permute-start.1 = (bf16[272,512]{1,0:T(8,128)(2,1)S(1)}, bf16[272,512]{1,0:T(8,128)(2,1)}, u32[]{:S(2)}, u32[]{:S(2)}) collective-permute-start(bf16[272,512]{1,0:T(8,128)(2,1)S(1)} %constant_dynamic-update-slice_fusion), channel_id=1, source_target_pairs={{0,1},{1,0},{2,3},{3,2},{4,5},{5,4},{6,7},{7,6},{8,9},{9,8},{10,11... | collective-permute-start | bytes 835592 | tf_op jit(solution)/shard_map/ppermute | solution.py:32
  22.6 5.0 %copy-start.1 = (bf16[272,1024]{1,0:T(8,128)(2,1)}, bf16[272,1024]{1,0:T(8,128)(2,1)S(1)}, u32[]{:S(2)}) copy-start(bf16[272,1024]{1,0:T(8,128)(2,1)S(1)} %multiply_convert_fusion) | copy-start | bytes 1671172
  31.0 6.4 %collective-permute-start.2 = (f32[96,256]{1,0:T(8,128)}, f32[96,256]{1,0:T(8,128)S(1)}, u32[]{:S(2)}, u32[]{:S(2)}) collective-permute-start(f32[96,256]{1,0:T(8,128)} %get-tuple-element.26.selected_ref), channel_id=1, source_target_pairs={{0,1},{1,0},{2,3},{3,2},{4,5},{5,4},{6,7},{7,6},{8,9},{9,8},{10,11... | collective-permute-start | bytes 294920 | tf_op jit(solution)/shard_map/ppermute | solution.py:32
  37.4 0.7 copy-start.13
  38.1 13.2 %copy-start.7 = (f32[16,1024]{1,0:T(8,128)S(1)}, f32[16,1024]{1,0:T(8,128)}, u32[]{:S(2)}) copy-start(f32[16,1024]{1,0:T(8,128)} %decay_log_ref.3) | copy-start | bytes 196612
  48.8 1.7 collective-permute-start.4
  52.9 6.7 %collective-permute-start.5 = (f32[40,1024]{1,0:T(8,128)}, f32[40,1024]{1,0:T(8,128)}, u32[]{:S(2)}, u32[]{:S(2)}) collective-permute-start(f32[40,1024]{1,0:T(8,128)} %pad_maximum_fusion.14), channel_id=1, source_target_pairs={{0,4},{2,6},{4,0},{6,2},{8,12},{10,14},{12,8},{14,10},{16,20},{18,... | collective-permute-start | bytes 491528 | tf_op jit(solution)/shard_map/ppermute | solution.py:32
  61.3 6.2 %collective-permute-start.7 = (f32[16,1024]{1,0:T(8,128)S(1)}, f32[16,1024]{1,0:T(8,128)S(1)}, u32[]{:S(2)}, u32[]{:S(2)}) collective-permute-start(f32[16,1024]{1,0:T(8,128)S(1)} %get-tuple-element.93), channel_id=1, source_target_pairs={{8,0},{10,2},{12,4},{14,6},{16,8},{18,10},{20,12},{22,14},{24,16},... | collective-permute-start | bytes 196616 | tf_op jit(solution)/shard_map/ppermute | solution.py:27
  62.6 6.4 %collective-permute-start.6 = (f32[16,1024]{1,0:T(8,128)S(1)}, f32[16,1024]{1,0:T(8,128)S(1)}, u32[]{:S(2)}, u32[]{:S(2)}) collective-permute-start(f32[16,1024]{1,0:T(8,128)S(1)} %get-tuple-element.94), channel_id=1, source_target_pairs={{0,8},{2,10},{4,12},{6,14},{8,16},{10,18},{12,20},{14,22},{16,24},... | collective-permute-start | bytes 196616 | tf_op jit(solution)/shard_map/ppermute | solution.py:27
  97.9 4.9 %collective-permute-start.9 = (f32[96,256]{1,0:T(8,128)}, f32[96,256]{1,0:T(8,128)S(1)}, u32[]{:S(2)}, u32[]{:S(2)}) collective-permute-start(f32[96,256]{1,0:T(8,128)} %get-tuple-element.32.select_grad_ref), channel_id=1, source_target_pairs={{0,1},{1,0},{2,3},{3,2},{4,5},{5,4},{6,7},{7,6},{8,9},{9,8},{10,11... | collective-permute-start | bytes 294920 | tf_op jit(solution)/shard_map/ppermute | solution.py:32
  102.8 0.6 copy-start.14
  103.5 8.8 %copy-start.12 = (bf16[1024,2,1024]{2,1,0:T(2,128)(2,1)S(1)}, bf16[1024,2,1024]{2,1,0:T(2,128)(2,1)}, u32[]{:S(2)}) copy-start(bf16[1024,2,1024]{2,1,0:T(2,128)(2,1)} %param.15) | copy-start | bytes 12582916
  108.2 3.9 %copy-start.10 = (f32[16,1024]{1,0:T(8,128)S(1)}, f32[16,1024]{1,0:T(8,128)}, u32[]{:S(2)}) copy-start(f32[16,1024]{1,0:T(8,128)} %get-tuple-element.36) | copy-start | bytes 196612
  108.2 4.1 %copy-start.4 = (bf16[256,1024]{1,0:T(8,128)(2,1)S(1)}, bf16[256,1024]{1,0:T(8,128)(2,1)}, u32[]{:S(2)}) copy-start(bf16[256,1024]{1,0:T(8,128)(2,1)} %get-tuple-element.37) | copy-start | bytes 1572868
  109.1 3.1 %collective-permute-start.10 = (f32[8,1024]{1,0:T(8,128)S(1)}, f32[8,1024]{1,0:T(8,128)S(1)}, u32[]{:S(2)}, u32[]{:S(2)}) collective-permute-start(f32[8,1024]{1,0:T(8,128)S(1)} %slice.225), channel_id=1, source_target_pairs={{2,0},{4,2},{6,4},{8,6},{10,8},{12,10},{14,12},{16,14},{18,16},{20... | collective-permute-start | bytes 98312 | tf_op jit(solution)/shard_map/ppermute | solution.py:27
  112.3 3.6 %copy-start.2 = (bf16[272,1024]{1,0:T(8,128)(2,1)S(1)}, bf16[272,1024]{1,0:T(8,128)(2,1)}, u32[]{:S(2)}) copy-start(bf16[272,1024]{1,0:T(8,128)(2,1)} %copy-done.1) | copy-start | bytes 1671172
  112.3 5.6 %copy-start.8 = (f32[112,1024]{1,0:T(8,128)S(1)}, f32[112,1024]{1,0:T(8,128)}, u32[]{:S(2)}) copy-start(f32[112,1024]{1,0:T(8,128)} %get-tuple-element.39) | copy-start | bytes 1376260
  112.3 5.6 %copy-start.9 = (f32[96,1024]{1,0:T(8,128)S(1)}, f32[96,1024]{1,0:T(8,128)}, u32[]{:S(2)}) copy-start(f32[96,1024]{1,0:T(8,128)} %get-tuple-element.38) | copy-start | bytes 1179652
  114.2 5.1 %copy-start.3 = (bf16[256,1024]{1,0:T(8,128)(2,1)S(1)}, bf16[256,1024]{1,0:T(8,128)(2,1)}, u32[]{:S(2)}) copy-start(bf16[256,1024]{1,0:T(8,128)(2,1)} %get-tuple-element.31) | copy-start | bytes 1572868
  114.2 3.7 %collective-permute-start.13 = (f32[1,1024]{1,0:T(1,128)S(1)}, f32[1,1024]{1,0:T(1,128)S(1)}, u32[]{:S(2)}, u32[]{:S(2)}) collective-permute-start(f32[1,1024]{1,0:T(1,128)S(1)} %bitcast.56), channel_id=1, source_target_pairs={{0,1},{1,0},{2,3},{3,2},{4,5},{5,4},{6,7},{7,6},{8,9},{9,8},{10,11... | collective-permute-start | bytes 12296 | tf_op jit(solution)/shard_map/ppermute | solution.py:32
  118.1 3.6 %collective-permute-start.14 = (bf16[128,1024]{1,0:T(8,128)(2,1)S(1)}, bf16[128,1024]{1,0:T(8,128)(2,1)S(1)}, u32[]{:S(2)}, u32[]{:S(2)}) collective-permute-start(bf16[128,1024]{1,0:T(8,128)(2,1)S(1)} %dynamic-slice_convert_fusion), channel_id=1, source_target_pairs={{0,2},{2,0},{4,6},{6,4},{8,10},{10,8},{12,14},{14,12},{16,18},{18,... | collective-permute-start | bytes 786440 | tf_op jit(solution)/shard_map/ppermute | solution.py:32
  120.1 35.5 %collective-permute-start.8 = (f32[256,512]{1,0:T(8,128)S(1)}, f32[256,512]{1,0:T(8,128)S(1)}, u32[]{:S(2)}, u32[]{:S(2)}) collective-permute-start(f32[256,512]{1,0:T(8,128)S(1)} %slice_select_fusion.1), channel_id=1, source_target_pairs={{0,1},{1,0},{2,3},{3,2},{4,5},{5,4},{6,7},{7,6},{8,9},{9,8},{10,11... | collective-permute-start | bytes 1572872 | tf_op jit(solution)/shard_map/ppermute | solution.py:32
  121.8 5.6 %collective-permute-start.15 = (bf16[64,1024]{1,0:T(8,128)(2,1)S(1)}, bf16[64,1024]{1,0:T(8,128)(2,1)S(1)}, u32[]{:S(2)}, u32[]{:S(2)}) collective-permute-start(bf16[64,1024]{1,0:T(8,128)(2,1)S(1)} %select_convert_fusion.9), channel_id=1, source_target_pairs={{0,4},{2,6},{4,0},{6,2},{8,12},{10,14},{12,8},{14,10},{16,20},{18,... | collective-permute-start | bytes 393224 | tf_op jit(solution)/shard_map/ppermute | solution.py:32
  127.5 4.3 %collective-permute-start.16 = (bf16[32,1024]{1,0:T(8,128)(2,1)S(1)}, bf16[32,1024]{1,0:T(8,128)(2,1)S(1)}, u32[]{:S(2)}, u32[]{:S(2)}) collective-permute-start(bf16[32,1024]{1,0:T(8,128)(2,1)S(1)} %select_convert_fusion.10), channel_id=1, source_target_pairs={{0,8},{2,10},{4,12},{6,14},{8,0},{10,2},{12,4},{14,6},{16,24},{18,... | collective-permute-start | bytes 196616 | tf_op jit(solution)/shard_map/ppermute | solution.py:32
  130.0 31.8 %collective-permute-start.30 = (bf16[512,1024]{1,0:T(8,128)(2,1)S(1)}, bf16[512,1024]{1,0:T(8,128)(2,1)S(1)}, u32[]{:S(2)}, u32[]{:S(2)}) collective-permute-start(bf16[512,1024]{1,0:T(8,128)(2,1)S(1)} %convolution_convert_fusion.1), channel_id=1, source_target_pairs={{0,2},{2,0},{4,6},{6,4},{8,10},{10,8},{12,14},{14,12},{16,18},{18,... | collective-permute-start | bytes 3145736 | tf_op jit(solution)/shard_map/ppermute | solution.py:32
  130.1 33.9 %collective-permute-start.38 = (bf16[512,1024]{1,0:T(8,128)(2,1)S(1)}, bf16[512,1024]{1,0:T(8,128)(2,1)S(1)}, u32[]{:S(2)}, u32[]{:S(2)}) collective-permute-start(bf16[512,1024]{1,0:T(8,128)(2,1)S(1)} %convolution_convert_fusion), channel_id=1, source_target_pairs={{0,2},{2,0},{4,6},{6,4},{8,10},{10,8},{12,14},{14,12},{16,18},{18,... | collective-permute-start | bytes 3145736 | tf_op jit(solution)/shard_map/ppermute | solution.py:32
  131.8 5.0 %collective-permute-start.17 = (bf16[16,1024]{1,0:T(8,128)(2,1)S(1)}, bf16[16,1024]{1,0:T(8,128)(2,1)S(1)}, u32[]{:S(2)}, u32[]{:S(2)}) collective-permute-start(bf16[16,1024]{1,0:T(8,128)(2,1)S(1)} %select_convert_fusion.11), channel_id=1, source_target_pairs={{0,16},{2,18},{4,20},{6,22},{8,24},{10,26},{12,28},{14,30},{16,0},... | collective-permute-start | bytes 98312 | tf_op jit(solution)/shard_map/ppermute | solution.py:32
  134.9 22.3 %copy-start.5 = (bf16[256,512]{1,0:T(8,128)(2,1)S(1)}, bf16[256,512]{1,0:T(8,128)(2,1)}, u32[]{:S(2)}) copy-start(bf16[256,512]{1,0:T(8,128)(2,1)} %param.13) | copy-start | bytes 786436
  134.9 22.3 %copy-start.6 = (bf16[256,512]{1,0:T(8,128)(2,1)S(1)}, bf16[256,512]{1,0:T(8,128)(2,1)}, u32[]{:S(2)}) copy-start(bf16[256,512]{1,0:T(8,128)(2,1)} %param.25) | copy-start | bytes 786436
  136.9 4.9 %collective-permute-start.18 = (bf16[16,1024]{1,0:T(8,128)(2,1)S(1)}, bf16[16,1024]{1,0:T(8,128)(2,1)S(1)}, u32[]{:S(2)}, u32[]{:S(2)}) collective-permute-start(bf16[16,1024]{1,0:T(8,128)(2,1)S(1)} %add_convert_fusion.3), channel_id=1, source_target_pairs={{0,16},{2,18},{4,20},{6,22},{8,24},{10,26},{12,28},{14,30},{16,0},... | collective-permute-start | bytes 98312 | tf_op jit(solution)/shard_map/ppermute | solution.py:32
  140.4 16.8 %collective-permute-start.11 = (f32[256,512]{1,0:T(8,128)S(1)}, f32[256,512]{1,0:T(8,128)S(1)}, u32[]{:S(2)}, u32[]{:S(2)}) collective-permute-start(f32[256,512]{1,0:T(8,128)S(1)} %slice_select_fusion), channel_id=1, source_target_pairs={{0,1},{1,0},{2,3},{3,2},{4,5},{5,4},{6,7},{7,6},{8,9},{9,8},{10,11... | collective-permute-start | bytes 1572872 | tf_op jit(solution)/shard_map/ppermute | solution.py:32
  141.8 9.6 %collective-permute-start.12 = (f32[256,1]{0,1:T(1,128)S(1)}, f32[256,1]{0,1:T(1,128)S(1)}, u32[]{:S(2)}, u32[]{:S(2)}) collective-permute-start(f32[256,1]{0,1:T(1,128)S(1)} %bitcast.63), channel_id=1, source_target_pairs={{0,1},{1,0},{2,3},{3,2},{4,5},{5,4},{6,7},{7,6},{8,9},{9,8},{10,11... | collective-permute-start | bytes 3080 | tf_op jit(solution)/shard_map/ppermute | solution.py:32
  151.3 4.3 %collective-permute-start.19 = (bf16[32,1024]{1,0:T(8,128)(2,1)S(1)}, bf16[32,1024]{1,0:T(8,128)(2,1)S(1)}, u32[]{:S(2)}, u32[]{:S(2)}) collective-permute-start(bf16[32,1024]{1,0:T(8,128)(2,1)S(1)} %pad_maximum_fusion.21), channel_id=1, source_target_pairs={{0,8},{2,10},{4,12},{6,14},{8,0},{10,2},{12,4},{14,6},{16,24},{18,... | collective-permute-start | bytes 196616 | tf_op jit(solution)/shard_map/ppermute | solution.py:32
  155.6 9.8 %collective-permute-start.22 = (bf16[512,1024]{1,0:T(8,128)(2,1)S(1)}, bf16[512,1024]{1,0:T(8,128)(2,1)S(1)}, u32[]{:S(2)}, u32[]{:S(2)}) collective-permute-start(bf16[512,1024]{1,0:T(8,128)(2,1)S(1)} %convolution_convert_fusion.2), channel_id=1, source_target_pairs={{0,2},{2,0},{4,6},{6,4},{8,10},{10,8},{12,14},{14,12},{16,18},{18,... | collective-permute-start | bytes 3145736 | tf_op jit(solution)/shard_map/ppermute | solution.py:32
  155.6 6.0 %collective-permute-start.20 = (bf16[64,1024]{1,0:T(8,128)(2,1)S(1)}, bf16[64,1024]{1,0:T(8,128)(2,1)S(1)}, u32[]{:S(2)}, u32[]{:S(2)}) collective-permute-start(bf16[64,1024]{1,0:T(8,128)(2,1)S(1)} %pad_maximum_fusion.20), channel_id=1, source_target_pairs={{0,4},{2,6},{4,0},{6,2},{8,12},{10,14},{12,8},{14,10},{16,20},{18,... | collective-permute-start | bytes 393224 | tf_op jit(solution)/shard_map/ppermute | solution.py:32
  161.7 3.4 %collective-permute-start.21 = (bf16[128,1024]{1,0:T(8,128)(2,1)S(1)}, bf16[128,1024]{1,0:T(8,128)(2,1)S(1)}, u32[]{:S(2)}, u32[]{:S(2)}) collective-permute-start(bf16[128,1024]{1,0:T(8,128)(2,1)S(1)} %pad_maximum_fusion.10), channel_id=1, source_target_pairs={{0,2},{2,0},{4,6},{6,4},{8,10},{10,8},{12,14},{14,12},{16,18},{18,... | collective-permute-start | bytes 786440 | tf_op jit(solution)/shard_map/ppermute | solution.py:32
  162.4 14.8 %collective-permute-start.31 = (bf16[256,1024]{1,0:T(8,128)(2,1)S(1)}, bf16[256,1024]{1,0:T(8,128)(2,1)S(1)}, u32[]{:S(2)}, u32[]{:S(2)}) collective-permute-start(bf16[256,1024]{1,0:T(8,128)(2,1)S(1)} %select_convert_fusion.1), channel_id=1, source_target_pairs={{0,4},{2,6},{4,0},{6,2},{8,12},{10,14},{12,8},{14,10},{16,20},{18,... | collective-permute-start | bytes 1572872 | tf_op jit(solution)/shard_map/ppermute | solution.py:32
  164.5 23.9 %collective-permute-start.39 = (bf16[256,1024]{1,0:T(8,128)(2,1)S(1)}, bf16[256,1024]{1,0:T(8,128)(2,1)S(1)}, u32[]{:S(2)}, u32[]{:S(2)}) collective-permute-start(bf16[256,1024]{1,0:T(8,128)(2,1)S(1)} %select_convert_fusion), channel_id=1, source_target_pairs={{0,4},{2,6},{4,0},{6,2},{8,12},{10,14},{12,8},{14,10},{16,20},{18,... | collective-permute-start | bytes 1572872 | tf_op jit(solution)/shard_map/ppermute | solution.py:32
  166.0 33.3 %collective-permute-start.23 = (bf16[256,1024]{1,0:T(8,128)(2,1)S(1)}, bf16[256,1024]{1,0:T(8,128)(2,1)S(1)}, u32[]{:S(2)}, u32[]{:S(2)}) collective-permute-start(bf16[256,1024]{1,0:T(8,128)(2,1)S(1)} %select_convert_fusion.2), channel_id=1, source_target_pairs={{0,4},{2,6},{4,0},{6,2},{8,12},{10,14},{12,8},{14,10},{16,20},{18,... | collective-permute-start | bytes 1572872 | tf_op jit(solution)/shard_map/ppermute | solution.py:32
  177.5 23.7 %collective-permute-start.32 = (bf16[128,1024]{1,0:T(8,128)(2,1)S(1)}, bf16[128,1024]{1,0:T(8,128)(2,1)S(1)}, u32[]{:S(2)}, u32[]{:S(2)}) collective-permute-start(bf16[128,1024]{1,0:T(8,128)(2,1)S(1)} %select_convert_fusion.4), channel_id=1, source_target_pairs={{0,8},{2,10},{4,12},{6,14},{8,0},{10,2},{12,4},{14,6},{16,24},{18,... | collective-permute-start | bytes 786440 | tf_op jit(solution)/shard_map/ppermute | solution.py:32
  188.7 13.0 %collective-permute-start.40 = (bf16[128,1024]{1,0:T(8,128)(2,1)S(1)}, bf16[128,1024]{1,0:T(8,128)(2,1)S(1)}, u32[]{:S(2)}, u32[]{:S(2)}) collective-permute-start(bf16[128,1024]{1,0:T(8,128)(2,1)S(1)} %select_convert_fusion.3), channel_id=1, source_target_pairs={{0,8},{2,10},{4,12},{6,14},{8,0},{10,2},{12,4},{14,6},{16,24},{18,... | collective-permute-start | bytes 786440 | tf_op jit(solution)/shard_map/ppermute | solution.py:32
  199.5 11.0 %collective-permute-start.24 = (bf16[128,1024]{1,0:T(8,128)(2,1)S(1)}, bf16[128,1024]{1,0:T(8,128)(2,1)S(1)}, u32[]{:S(2)}, u32[]{:S(2)}) collective-permute-start(bf16[128,1024]{1,0:T(8,128)(2,1)S(1)} %select_convert_fusion.5), channel_id=1, source_target_pairs={{0,8},{2,10},{4,12},{6,14},{8,0},{10,2},{12,4},{14,6},{16,24},{18,... | collective-permute-start | bytes 786440 | tf_op jit(solution)/shard_map/ppermute | solution.py:32
  201.3 13.0 %collective-permute-start.33 = (bf16[64,1024]{1,0:T(8,128)(2,1)S(1)}, bf16[64,1024]{1,0:T(8,128)(2,1)S(1)}, u32[]{:S(2)}, u32[]{:S(2)}) collective-permute-start(bf16[64,1024]{1,0:T(8,128)(2,1)S(1)} %select_convert_fusion.7), channel_id=1, source_target_pairs={{0,16},{2,18},{4,20},{6,22},{8,24},{10,26},{12,28},{14,30},{16,0},... | collective-permute-start | bytes 393224 | tf_op jit(solution)/shard_map/ppermute | solution.py:32
  201.8 23.7 %collective-permute-start.41 = (bf16[64,1024]{1,0:T(8,128)(2,1)S(1)}, bf16[64,1024]{1,0:T(8,128)(2,1)S(1)}, u32[]{:S(2)}, u32[]{:S(2)}) collective-permute-start(bf16[64,1024]{1,0:T(8,128)(2,1)S(1)} %select_convert_fusion.6), channel_id=1, source_target_pairs={{0,16},{2,18},{4,20},{6,22},{8,24},{10,26},{12,28},{14,30},{16,0},... | collective-permute-start | bytes 393224 | tf_op jit(solution)/shard_map/ppermute | solution.py:32
  210.7 20.4 %collective-permute-start.25 = (bf16[64,1024]{1,0:T(8,128)(2,1)S(1)}, bf16[64,1024]{1,0:T(8,128)(2,1)S(1)}, u32[]{:S(2)}, u32[]{:S(2)}) collective-permute-start(bf16[64,1024]{1,0:T(8,128)(2,1)S(1)} %select_convert_fusion.8), channel_id=1, source_target_pairs={{0,16},{2,18},{4,20},{6,22},{8,24},{10,26},{12,28},{14,30},{16,0},... | collective-permute-start | bytes 393224 | tf_op jit(solution)/shard_map/ppermute | solution.py:32
  214.4 19.6 %collective-permute-start.34 = (bf16[64,1024]{1,0:T(8,128)(2,1)S(1)}, bf16[64,1024]{1,0:T(8,128)(2,1)S(1)}, u32[]{:S(2)}, u32[]{:S(2)}) collective-permute-start(bf16[64,1024]{1,0:T(8,128)(2,1)S(1)} %add_convert_fusion.1), channel_id=1, source_target_pairs={{0,16},{2,18},{4,20},{6,22},{8,24},{10,26},{12,28},{14,30},{16,0},... | collective-permute-start | bytes 393224 | tf_op jit(solution)/shard_map/ppermute | solution.py:32
  225.6 11.1 %collective-permute-start.42 = (bf16[64,1024]{1,0:T(8,128)(2,1)S(1)}, bf16[64,1024]{1,0:T(8,128)(2,1)S(1)}, u32[]{:S(2)}, u32[]{:S(2)}) collective-permute-start(bf16[64,1024]{1,0:T(8,128)(2,1)S(1)} %add_convert_fusion), channel_id=1, source_target_pairs={{0,16},{2,18},{4,20},{6,22},{8,24},{10,26},{12,28},{14,30},{16,0},... | collective-permute-start | bytes 393224 | tf_op jit(solution)/shard_map/ppermute | solution.py:32
  231.2 6.9 %collective-permute-start.26 = (bf16[64,1024]{1,0:T(8,128)(2,1)S(1)}, bf16[64,1024]{1,0:T(8,128)(2,1)S(1)}, u32[]{:S(2)}, u32[]{:S(2)}) collective-permute-start(bf16[64,1024]{1,0:T(8,128)(2,1)S(1)} %add_convert_fusion.2), channel_id=1, source_target_pairs={{0,16},{2,18},{4,20},{6,22},{8,24},{10,26},{12,28},{14,30},{16,0},... | collective-permute-start | bytes 393224 | tf_op jit(solution)/shard_map/ppermute | solution.py:32
  234.0 17.3 %collective-permute-start.35 = (bf16[128,1024]{1,0:T(8,128)(2,1)S(1)}, bf16[128,1024]{1,0:T(8,128)(2,1)S(1)}, u32[]{:S(2)}, u32[]{:S(2)}) collective-permute-start(bf16[128,1024]{1,0:T(8,128)(2,1)S(1)} %pad_maximum_fusion.12), channel_id=1, source_target_pairs={{0,8},{2,10},{4,12},{6,14},{8,0},{10,2},{12,4},{14,6},{16,24},{18,... | collective-permute-start | bytes 786440 | tf_op jit(solution)/shard_map/ppermute | solution.py:32
  236.8 12.6 %collective-permute-start.43 = (bf16[128,1024]{1,0:T(8,128)(2,1)S(1)}, bf16[128,1024]{1,0:T(8,128)(2,1)S(1)}, u32[]{:S(2)}, u32[]{:S(2)}) collective-permute-start(bf16[128,1024]{1,0:T(8,128)(2,1)S(1)} %pad_maximum_fusion.13), channel_id=1, source_target_pairs={{0,8},{2,10},{4,12},{6,14},{8,0},{10,2},{12,4},{14,6},{16,24},{18,... | collective-permute-start | bytes 786440 | tf_op jit(solution)/shard_map/ppermute | solution.py:32
  238.2 16.7 %collective-permute-start.27 = (bf16[128,1024]{1,0:T(8,128)(2,1)S(1)}, bf16[128,1024]{1,0:T(8,128)(2,1)S(1)}, u32[]{:S(2)}, u32[]{:S(2)}) collective-permute-start(bf16[128,1024]{1,0:T(8,128)(2,1)S(1)} %pad_maximum_fusion.11), channel_id=1, source_target_pairs={{0,8},{2,10},{4,12},{6,14},{8,0},{10,2},{12,4},{14,6},{16,24},{18,... | collective-permute-start | bytes 786440 | tf_op jit(solution)/shard_map/ppermute | solution.py:32
  249.5 14.9 %collective-permute-start.44 = (bf16[256,1024]{1,0:T(8,128)(2,1)S(1)}, bf16[256,1024]{1,0:T(8,128)(2,1)S(1)}, u32[]{:S(2)}, u32[]{:S(2)}) collective-permute-start(bf16[256,1024]{1,0:T(8,128)(2,1)S(1)} %pad_maximum_fusion.9), channel_id=1, source_target_pairs={{0,4},{2,6},{4,0},{6,2},{8,12},{10,14},{12,8},{14,10},{16,20},{18,... | collective-permute-start | bytes 1572872 | tf_op jit(solution)/shard_map/ppermute | solution.py:32
  251.5 24.1 %collective-permute-start.36 = (bf16[256,1024]{1,0:T(8,128)(2,1)S(1)}, bf16[256,1024]{1,0:T(8,128)(2,1)S(1)}, u32[]{:S(2)}, u32[]{:S(2)}) collective-permute-start(bf16[256,1024]{1,0:T(8,128)(2,1)S(1)} %pad_maximum_fusion.8), channel_id=1, source_target_pairs={{0,4},{2,6},{4,0},{6,2},{8,12},{10,14},{12,8},{14,10},{16,20},{18,... | collective-permute-start | bytes 1572872 | tf_op jit(solution)/shard_map/ppermute | solution.py:32
  255.1 30.8 %collective-permute-start.28 = (bf16[256,1024]{1,0:T(8,128)(2,1)S(1)}, bf16[256,1024]{1,0:T(8,128)(2,1)S(1)}, u32[]{:S(2)}, u32[]{:S(2)}) collective-permute-start(bf16[256,1024]{1,0:T(8,128)(2,1)S(1)} %pad_maximum_fusion.7), channel_id=1, source_target_pairs={{0,4},{2,6},{4,0},{6,2},{8,12},{10,14},{12,8},{14,10},{16,20},{18,... | collective-permute-start | bytes 1572872 | tf_op jit(solution)/shard_map/ppermute | solution.py:32
  264.7 23.0 %collective-permute-start.45 = (bf16[512,1024]{1,0:T(8,128)(2,1)S(1)}, bf16[512,1024]{1,0:T(8,128)(2,1)S(1)}, u32[]{:S(2)}, u32[]{:S(2)}) collective-permute-start(bf16[512,1024]{1,0:T(8,128)(2,1)S(1)} %pad_maximum_fusion.4), channel_id=1, source_target_pairs={{0,2},{2,0},{4,6},{6,4},{8,10},{10,8},{12,14},{14,12},{16,18},{18,... | collective-permute-start | bytes 3145736 | tf_op jit(solution)/shard_map/ppermute | solution.py:32
  276.0 14.8 %collective-permute-start.37 = (bf16[512,1024]{1,0:T(8,128)(2,1)S(1)}, bf16[512,1024]{1,0:T(8,128)(2,1)S(1)}, u32[]{:S(2)}, u32[]{:S(2)}) collective-permute-start(bf16[512,1024]{1,0:T(8,128)(2,1)S(1)} %pad_maximum_fusion.3), channel_id=1, source_target_pairs={{0,2},{2,0},{4,6},{6,4},{8,10},{10,8},{12,14},{14,12},{16,18},{18,... | collective-permute-start | bytes 3145736 | tf_op jit(solution)/shard_map/ppermute | solution.py:32
  286.4 4.9 %collective-permute-start.29 = (bf16[512,1024]{1,0:T(8,128)(2,1)S(1)}, bf16[512,1024]{1,0:T(8,128)(2,1)S(1)}, u32[]{:S(2)}, u32[]{:S(2)}) collective-permute-start(bf16[512,1024]{1,0:T(8,128)(2,1)S(1)} %pad_maximum_fusion.2), channel_id=1, source_target_pairs={{0,2},{2,0},{4,6},{6,4},{8,10},{10,8},{12,14},{14,12},{16,18},{18,... | collective-permute-start | bytes 3145736 | tf_op jit(solution)/shard_map/ppermute | solution.py:32

commit v3 on v2

--- a/solution.py
+++ b/solution.py
@@ -40,21 +40,42 @@
     return bits
 
 
-def summed_over_wide(keep, send):
-    place = lax.axis_index("wide")
-    bits = wide_bits()
-    piece = keep + swapped(send.astype(bf16), "wide", bits[0]).astype(f32)
-    for bit in bits[1:]:
-        upper = (place & bit) != 0
-        half = piece.shape[0] // 2
-        low, high = piece[:half], piece[half:]
-        away = jnp.where(upper, low, high).astype(bf16)
-        piece = jnp.where(upper, high, low) + swapped(away, "wide", bit).astype(f32)
-    held = piece.astype(bf16)
+def to_next_both(array):
+    count, sides = lax.axis_size("wide"), lax.axis_size("narrow")
+    pairs = [
+        (i * sides + k, (i + 1) * sides + (sides - 1 - k))
+        for i in range(count - 1)
+        for k in range(sides)
+    ]
+    return passed_along(array, "wide", 1), lax.ppermute(array, ("wide", "narrow"), pairs)
+
+
+def is_upper(bit):
+    return (lax.axis_index("wide") & bit) != 0
+
+
+def scatter_step(piece, bit):
+    half = piece.shape[0] // 2
+    low, high = piece[:half], piece[half:]
+    away = jnp.where(is_upper(bit), low, high).astype(bf16)
+    return jnp.where(is_upper(bit), high, low) + swapped(away, "wide", bit).astype(f32)
+
+
+def gather_step(held, bit):
+    other = swapped(held, "wide", bit)
+    upper = is_upper(bit)
+    return jnp.concatenate([jnp.where(upper, other, held), jnp.where(upper, held, other)])
+
+
+def scattered(piece, bits):
+    for bit in bits:
+        piece = scatter_step(piece, bit)
+    return piece.astype(bf16)
+
+
+def gathered(held, bits):
     for bit in reversed(bits):
-        upper = (place & bit) != 0
-        other = swapped(held, "wide", bit)
-        held = jnp.concatenate([jnp.where(upper, other, held), jnp.where(upper, held, other)])
+        held = gather_step(held, bit)
     return held
 
 
@@ -67,11 +88,24 @@
     )
 
 
-def weight_sum(left, right):
-    mine, other = halves_of(left, 1)
-    send = lax.dot_general(other, right, contract_first, preferred_element_type=f32)
-    keep = lax.dot_general(mine, right, contract_first, preferred_element_type=f32)
-    return summed_over_wide(keep, send)
+def packed_rows(product):
+    half = product.shape[0] // 2
+    return jnp.concatenate([product[:half], product[half:]], axis=1)
+
+
+def times(left, right):
+    return lax.dot_general(left, right, contract_first, preferred_element_type=f32)
+
+
+def first_step(parts):
+    mine, send = [], []
+    for left, right, pack in parts:
+        own, other = halves_of(left, 1)
+        keep_product, send_product = times(own, right), times(other, right)
+        mine.append(packed_rows(keep_product) if pack else keep_product)
+        send.append(packed_rows(send_product) if pack else send_product)
+    away = jnp.concatenate(send).astype(bf16)
+    return jnp.concatenate(mine) + swapped(away, "wide", 1).astype(f32)
 
 
 def silu_slope(values):
@@ -83,12 +117,12 @@
     return jnp.maximum(values, 0.0) + jnp.log1p(jnp.exp(-jnp.abs(values)))
 
 
-def column_spec(rows, width=scan_width):
-    return pl.BlockSpec((rows, width), lambda j: (0, j))
-
-
-def part_spec(part, rows, width=scan_width):
-    return pl.BlockSpec((None, rows, width), lambda j: (part, 0, j))
+def column_spec(rows, start=0):
+    return pl.BlockSpec((rows, scan_width), lambda j: (0, start + j))
+
+
+def part_spec(part, rows, start=0):
+    return pl.BlockSpec((None, rows, scan_width), lambda j: (part, 0, start + j))
 
 
 def whole_spec(rows, width):
@@ -123,7 +157,8 @@
 ):
     rows = act_ref.shape[0]
     taps = conv_weight_ref.shape[0]
-    inner[...] = inner_ref[...].astype(f32)
+    inner[:halo, :] = inner_ref[rows:, :].astype(f32)
+    inner[halo:, :] = inner_ref[:rows, :].astype(f32)
     total = conv_bias_ref[...] + conv_weight_ref[taps - 1 :, :] * inner[halo:, :]
     for lag in range(1, taps):
         earlier = inner[pl.ds(halo - lag, rows), :] * mask_ref[:, lag : lag + 1]
@@ -238,9 +273,9 @@
 
 
 def scan_ends(
-    selected, other, step_weight, step_bias, act, projected, gated_grad, masks, decay_log
+    part, selected, other, step_weight, step_bias, act, projected, gated_grad, masks, decay_log
 ):
-    rows, width = act.shape
+    rows, width = act.shape[0], scan_width
     count = decay_log.shape[0]
     columns = selected.shape[0]
     rank = step_weight.shape[0]
@@ -251,13 +286,13 @@
         [
             whole_spec(columns, rows),
             whole_spec(columns, rows),
-            column_spec(rank),
-            column_spec(1),
-            column_spec(rows),
-            pl.BlockSpec((None, rows, scan_width), lambda j: (0, 0, j)),
-            column_spec(rows),
+            column_spec(rank, part),
+            column_spec(1, part),
+            column_spec(rows, part),
+            part_spec(1, rows, part),
+            column_spec(rows, part),
             whole_spec(rows, masks.shape[1]),
-            column_spec(count),
+            column_spec(count, part),
         ],
         [column_spec(rows), column_spec(rows), column_spec(2 * count + 8)],
         [
@@ -266,7 +301,7 @@
             jax.ShapeDtypeStruct((2 * count + 8, width), f32),
         ],
         [pltpu.VMEM((2 * count, rows), f32)] + [pltpu.VMEM((rows, scan_width), f32)] * 3,
-        10_000_000_000,
+        5_000_000_000,
         selected,
         other,
         step_weight,
@@ -328,6 +363,8 @@
     tail_ref,
     skip_ref,
     step_weight_ref,
+    before_ref,
+    after_ref,
     gated_ref,
     gate_grad_ref,
     act_grad_ref,
@@ -350,8 +387,6 @@
     count = decay_log_ref.shape[0]
     rank = step_weight_ref.shape[0]
     blocks = rows // body_rows
-    first = pl.program_id(0) == 0
-    last = pl.program_id(0) == pl.num_programs(0) - 1
     decay = -jnp.exp(decay_log_ref[...])
     decay2 = decay * log2e
     selected = selected_ref[...] + other_ref[...]
@@ -362,12 +397,6 @@
     held_step[...] = jnp.where(mask_ref[:, 1:2] > 0.0, step, reset_step)
     drive[...] = step * act
     states[:count, :] = entry_ref[...]
-
-    @pl.when(first)
-    def _():
-        in_sum[...] = jnp.zeros(in_sum.shape, f32)
-        read_sum[...] = jnp.zeros(read_sum.shape, f32)
-        select_grad_ref[...] = jnp.zeros(select_grad_ref.shape, f32)
 
     def at_token(t):
         return pl.ds(pl.multiple_of(t * count, count), count)
@@ -408,8 +437,8 @@
             row = pl.ds(t, 1)
             grad = scan_grad[row, :]
             summed = columns[count:, i : i + 1] * grad + adjoint
-            read_sum[at_token(t), :] += tree_sum(lane_tiles(grad * states[at_token(t + 1), :]))
-            in_sum[at_token(t), :] += tree_sum(lane_tiles(summed * drive[row, :]))
+            read_sum[at_token(t), :] = tree_sum(lane_tiles(grad * states[at_token(t + 1), :]))
+            in_sum[at_token(t), :] = tree_sum(lane_tiles(summed * drive[row, :]))
             keep_halves(halves, i, summed * columns[:count, i : i + 1])
             adjoint = factors[at_token(t), :] * summed
             held = adjoint * states[at_token(t), :]
@@ -431,19 +460,19 @@
     small_ref[rank + count + 1 : rank + count + 2, :] = bias_grad
     spare = small_ref.shape[0] - (rank + count + 2)
     small_ref[rank + count + 2 :, :] = jnp.zeros((spare, small_ref.shape[1]), f32)
-    select_grad_ref[:rank, :] += lax.dot_general(
+    before = before_ref[...]
+    select_grad_ref[:rank, :] = before[:rank] + lax.dot_general(
         step_weight_ref[...], pre_grad, contract_last, preferred_element_type=f32
     )
-
-    @pl.when(last)
-    def _():
-        for n in range(count):
-            at = pl.ds(n, rows, stride=count)
-            select_grad_ref[rank + n : rank + n + 1, :] = lane_sums(in_sum[at, :])
-            select_grad_ref[rank + count + n : rank + count + n + 1, :] = lane_sums(read_sum[at, :])
+    for n in range(count):
+        at = pl.ds(n, rows, stride=count)
+        low, high = rank + n, rank + count + n
+        select_grad_ref[low : low + 1, :] = before[low : low + 1] + lane_sums(in_sum[at, :])
+        select_grad_ref[high : high + 1, :] = before[high : high + 1] + lane_sums(read_sum[at, :])
 
 
 def scan_full(
+    part,
     selected,
     other,
     step_pre,
@@ -457,6 +486,8 @@
     tail,
     skip_gain,
     step_weight,
+    before,
+    after,
 ):
     rows, width = step.shape
     count = decay_log.shape[0]
@@ -473,15 +504,17 @@
             whole_spec(columns, rows),
             column_spec(rows),
             column_spec(rows),
-            column_spec(rows),
-            pl.BlockSpec((None, rows, scan_width), lambda j: (0, 0, j)),
-            column_spec(rows),
+            column_spec(rows, part),
+            part_spec(1, rows, part),
+            column_spec(rows, part),
             whole_spec(rows, masks.shape[1]),
+            column_spec(count, part),
             column_spec(count),
             column_spec(count),
-            column_spec(count),
-            column_spec(1),
-            column_spec(rank),
+            column_spec(1, part),
+            column_spec(rank, part),
+            whole_spec(columns, rows),
+            pl.BlockSpec(memory_space=pl.ANY),
         ],
         [column_spec(rows)] * 3 + [whole_spec(columns, rows), column_spec(small)],
         [
@@ -501,7 +534,7 @@
             pltpu.VMEM((rows * count, lanes), f32),
             pltpu.VMEM((rows * count, lanes), f32),
         ],
-        24_000_000_000,
+        13_000_000_000,
         selected,
         other,
         step_pre,
@@ -515,6 +548,8 @@
         tail,
         skip_gain,
         step_weight,
+        before,
+        after,
     )
 
 
@@ -543,7 +578,8 @@
     )
     conv_grad = total * silu_slope(convolved_ref[...])
     small_ref[:columns, :] = jnp.dot(select_grad, act_ref[...], preferred_element_type=f32)
-    inner[...] = inner_ref[...].astype(f32)
+    inner[:halo, :] = inner_ref[rows:, :].astype(f32)
+    inner[halo:, :] = inner_ref[:rows, :].astype(f32)
     edges = jnp.zeros((8, conv_grad.shape[1]), f32)
     shifted[:8, :] = edges
     shifted[rows + 8 :, :] = edges
@@ -571,9 +607,9 @@
 
 
 def convolve_grad(
-    select_grad, other, select_weight, act_grad, convolved, act, projected, conv_weight, masks
+    part, select_grad, other, select_weight, act_grad, convolved, act, projected, conv_weight, masks
 ):
-    rows, width = act.shape
+    rows, width = act_grad.shape
     extended = rows + halo
     columns = select_weight.shape[0]
     taps = conv_weight.shape[0]
@@ -585,12 +621,12 @@
         [
             whole_spec(columns, rows),
             whole_spec(columns, rows),
-            column_spec(columns),
+            column_spec(columns, part),
             column_spec(rows),
-            column_spec(rows),
-            column_spec(rows),
-            part_spec(0, extended),
-            column_spec(taps),
+            column_spec(rows, part),
+            column_spec(rows, part),
+            part_spec(0, extended, part),
+            column_spec(taps, part),
             whole_spec(rows, masks.shape[1]),
         ],
         [column_spec(rows), column_spec(16), column_spec(small)],
@@ -600,7 +636,7 @@
             jax.ShapeDtypeStruct((small, width), f32),
         ],
         [pltpu.VMEM((extended, scan_width), f32), pltpu.VMEM((rows + 16, scan_width), f32)],
-        6_000_000_000,
+        3_000_000_000,
         select_grad,
         other,
         select_weight,
@@ -613,24 +649,65 @@
     )
 
 
-def join_kernel(inner_ref, gate_ref, out_ref):
-    out_ref[:, 0, :] = inner_ref[...].astype(f32)
-    out_ref[:, 1, :] = gate_ref[...].astype(f32)
-
-
-def joined(inner, gate):
-    depth, width = inner.shape
-    rows = 256
-    spec = pl.BlockSpec((rows, width), lambda j: (j, 0))
+def normalize_kernel(
+    own_ref, other_ref, edge_ref, other_edge_ref, gain_ref, whole_ref, normed_ref, inverse_ref
+):
+    rows, half = own_ref.shape
+    right = lax.axis_index("narrow") == 1
+    for at, own, other in ((0, own_ref, other_ref), (rows, edge_ref, other_edge_ref)):
+        end = at + own.shape[0]
+        whole_ref[at:end, :half] = jnp.where(right, other[...], own[...])
+        whole_ref[at:end, half:] = jnp.where(right, own[...], other[...])
+    whole = whole_ref[...].astype(f32)
+    inverse = lax.rsqrt(jnp.mean(whole * whole, axis=1, keepdims=True) + epsilon)
+    normed_ref[...] = (whole * inverse * gain_ref[...]).astype(bf16)
+    inverse_ref[...] = inverse[:rows]
+
+
+def normalized(own, other, edge, other_edge, gain):
+    rows, half = own.shape
+    extended = rows + edge.shape[0]
+    return pl.pallas_call(
+        normalize_kernel,
+        out_shape=[
+            jax.ShapeDtypeStruct((extended, 2 * half), bf16),
+            jax.ShapeDtypeStruct((extended, 2 * half), bf16),
+            jax.ShapeDtypeStruct((rows, 1), f32),
+        ],
+        name="normalized",
+    )(own, other, edge, other_edge, gain)
+
+
+def join_kernel(first_ref, second_ref, inner_ref, out_ref):
+    half = scan_width
+    step = pl.program_id(0)
+    rows = first_ref.shape[0]
+    core_rows = inner_ref.shape[0] // 2
+    out_ref[:, 1, :half] = first_ref[...].astype(f32)
+    out_ref[:, 1, half:] = second_ref[...].astype(f32)
+    for k in range(4):
+
+        @pl.when(step == k)
+        def _():
+            at, lane = (k // 2) * core_rows, (k % 2) * half
+            for part in range(2):
+                block = inner_ref[at + part * rows : at + (part + 1) * rows, lane : lane + half]
+                out_ref[:, 0, part * half : (part + 1) * half] = block.astype(f32)
+
+
+def joined(first, second, inner):
+    depth = first.shape[0]
+    rows = depth // 4
+    spec = pl.BlockSpec((rows, scan_width), lambda j: (1 + 2 * (j // 2), j % 2))
     return pl.pallas_call(
         join_kernel,
-        grid=(depth // rows,),
-        in_specs=[spec, spec],
-        out_specs=pl.BlockSpec((rows, 2, width), lambda j: (j, 0, 0)),
-        out_shape=jax.ShapeDtypeStruct((depth, 2, width), f32),
+        grid=(4,),
+        in_specs=[spec, spec, whole_spec(*inner.shape)],
+        out_specs=pl.BlockSpec((rows, 2, 2 * scan_width), lambda j: (j, 0, 0)),
+        out_shape=jax.ShapeDtypeStruct((depth, 2, 2 * scan_width), f32),
         compiler_params=pltpu.CompilerParams(vmem_limit_bytes=vmem_bytes),
         name="joined",
-    )(inner, gate)
+    )(first, second, inner)
 
 
 def carried(ends, decay):
@@ -697,13 +774,11 @@
             [jnp.where(right_half, other, own), jnp.where(right_half, own, other)], axis=1
         )
 
-    last_ids = segment_ids[rows - halo :]
-    same_as_last = (last_ids == segment_ids[rows - 1 :])[:, None]
+    other_tokens = swapped(tokens, "narrow", 1)
+    other_cot = swapped(cotangent, "narrow", 1)
+    same_as_last = (segment_ids[rows - halo :] == segment_ids[rows - 1 :])[:, None]
     edge_rows = jnp.where(same_as_last, tokens[rows - halo :], jnp.zeros((), tokens.dtype))
-    before_own = passed_along(edge_rows, "wide", 1)
-    sent = jnp.concatenate([before_own, tokens])
-    whole_ext = both_halves(sent, swapped(sent, "narrow", 1)).astype(f32)
-    cot_whole = both_halves(cotangent, swapped(cotangent, "narrow", 1))
+    edge, other_edge = to_next_both(edge_rows)
 
     padded_ids = jnp.concatenate([jnp.broadcast_to(segment_ids[:1], (taps - 1,)), segment_ids])
     masks = jnp.stack(
@@ -714,51 +789,71 @@
         + [jnp.zeros((rows,), f32)] * (8 - taps),
         axis=1,
     )
-
-    inverse_ext = lax.rsqrt(jnp.mean(whole_ext * whole_ext, axis=1, keepdims=True) + epsilon)
-    normed_ext = (whole_ext * inverse_ext * norm_gain).astype(bf16)
+    whole_ext, normed_ext, inverse = normalized(
+        tokens, other_tokens, edge, other_edge, norm_gain[None]
+    )
     projected = jnp.einsum(
         "td,dce->cte", normed_ext, in_weight, preferred_element_type=f32
     ).astype(bf16)
-    gate_half = projected[1:, halo:]
     convolved, act, selected = convolve(
         projected, conv_weight, conv_bias[None], select_weight, masks
     )
     other_selected = swapped(selected, "narrow", 1)
+    cot_whole = both_halves(cotangent, other_cot)
     gated_grad = lax.dot_general(
         cot_whole, out_weight, contract_last, preferred_element_type=f32
     )
-    step_pre, step, ends = scan_ends(
-        selected,
-        other_selected,
-        step_weight,
-        step_bias[None],
-        act,
-        gate_half,
-        gated_grad,
-        masks,
-        decay_log,
-    )
-    entry, tail = carried(ends, -jnp.exp(decay_log))
-    gated, gate_grad, act_grad, select_grad, scan_small = scan_full(
-        selected,
-        other_selected,
-        step_pre,
-        step,
-        act,
-        gate_half,
-        gated_grad,
-        masks,
-        decay_log,
-        entry,
-        tail,
-        skip_gain[None],
-        step_weight,
-    )
+    parts = range(out_weight.shape[0] // scan_width)
+    decay = -jnp.exp(decay_log)
+    started = []
+    for part in parts:
+        step_pre, step, ends = scan_ends(
+            part,
+            selected,
+            other_selected,
+            step_weight,
+            step_bias[None],
+            act,
+            projected,
+            gated_grad,
+            masks,
+            decay_log,
+        )
+        here = decay[:, part * scan_width : (part + 1) * scan_width]
+        started.append((step_pre, step, carried(ends, here)))
+    normed = normed_ext[:rows]
+    bits = wide_bits()
+    select_grad = jnp.zeros(selected.shape, f32)
+    waited = select_grad
+    done, sums = [], []
+    for part in parts:
+        step_pre, step, (entry, tail) = started[part]
+        gated, gate_grad, act_grad, select_grad, small = scan_full(
+            part,
+            selected,
+            other_selected,
+            step_pre,
+            step,
+            act,
+            projected,
+            gated_grad,
+            masks,
+            decay_log,
+            entry,
+            tail,
+            skip_gain[None],
+            step_weight,
+            select_grad,
+            waited,
+        )
+        done.append((gated, gate_grad, act_grad, small))
+        waited = first_step([(gated, cot_whole, False), (normed, gate_grad, True)])
+        sums.append(waited)
     other_select_grad = swapped(select_grad, "narrow", 1)
-    out_weight_grad = weight_sum(gated, cot_whole)
-    normed = normed_ext[halo:]
-    gate_weight_grad = weight_sum(normed, gate_grad)
+    sums = [gathered(scattered(piece, bits[1:]), bits) for piece in sums]
+    gated, gate_grad, _, scan_small = [
+        jnp.concatenate(pieces, axis=1) for pieces in zip(*done)
+    ]
 
     def narrow_halves(array):
         low, high = array[:, :features], array[:, features:]
@@ -769,29 +864,47 @@
     out_sum = out_mine + swapped(out_other, "narrow", 1)
     layer_out = (tokens.astype(f32) + out_sum).astype(bf16)
 
-    inner_main, edges, conv_small = convolve_grad(
-        select_grad,
-        other_select_grad,
-        select_weight,
-        act_grad,
-        convolved,
-        act,
-        projected,
-        conv_weight,
-        masks,
-    )
+    results = [
+        convolve_grad(
+            part,
+            select_grad,
+            other_select_grad,
+            select_weight,
+            done[part][2],
+            convolved,
+            act,
+            projected,
+            conv_weight,
+            masks,
+        )
+        for part in parts
+    ]
+    inner_main, edges, conv_small = [jnp.concatenate(x, axis=1) for x in zip(*results)]
     from_next = passed_along(edges[:8], "wide", -1)
     last_rows = edges[8:] + jnp.where(same_as_last[halo - 8 :], from_next, 0.0)
     inner_grad = jnp.concatenate([inner_main[: rows - 8], last_rows.astype(bf16)])
+    inner_piece = first_step(
+        [
+            (normed, inner_grad[:, part * scan_width : (part + 1) * scan_width], True)
+            for part in parts
+        ]
+    )
     normed_part = jnp.einsum(
         "cte,dce->td", jnp.stack([inner_grad, gate_grad]), in_weight, preferred_element_type=f32
     )
-    inner_weight_grad = weight_sum(normed, inner_grad)
-
-    whole = whole_ext[halo:]
-    inverse = inverse_ext[halo:]
+    whole = whole_ext[:rows].astype(f32)
     gain_part = jnp.sum(normed_part * whole * inverse, axis=0, keepdims=True)
     row_part = jnp.sum(normed_part * norm_gain * whole, axis=1, keepdims=True)
+
+    spare = -(scan_small.shape[0] + conv_small.shape[0] + 1) % 256
+    small = jnp.concatenate(
+        [scan_small, conv_small, gain_part, jnp.zeros((spare, gain_part.shape[1]), f32)]
+    )
+    small_mine, small_other = halves_of(small, 0)
+    small_piece = small_mine + swapped(small_other.astype(bf16), "wide", 1).astype(f32)
+    last_piece = scattered(jnp.concatenate([inner_piece, small_piece]), bits[1:])
+    inner_sum = gathered(last_piece, bits)
+
     normed_mine, normed_other = narrow_halves(normed_part)
     row_sum = row_part + swapped(row_part, "narrow", 1)
     normed_sum = normed_mine + swapped(normed_other, "narrow", 1)
@@ -801,20 +914,25 @@
     ) * (row_sum / (2 * features))
     tokens_grad = (whole_grad + cotangent.astype(f32)).astype(bf16)
 
-    gain_sum = gain_part + swapped(gain_part, "narrow", 1)
-    spare = -(scan_small.shape[0] + conv_small.shape[0] + 1) % 256
-    small = jnp.concatenate(
-        [scan_small, conv_small, gain_sum, jnp.zeros((spare, gain_sum.shape[1]), f32)]
-    )
-    small_sum = summed_over_wide(*halves_of(small, 0)).astype(f32)
+    core_rows = inner_sum.shape[0] // 2
+    small_at = inner_piece.shape[0]
+    small_sum = jnp.concatenate(
+        [inner_sum[small_at:core_rows], inner_sum[core_rows + small_at :]]
+    ).astype(f32)
     scan_sum = small_sum[: scan_small.shape[0]]
     conv_sum = small_sum[scan_small.shape[0] : scan_small.shape[0] + conv_small.shape[0]]
-    norm_gain_grad = small_sum[scan_small.shape[0] + conv_small.shape[0]]
+    gain_row = scan_small.shape[0] + conv_small.shape[0]
+    gain_sum = small_sum[gain_row : gain_row + 1]
+    norm_gain_grad = (gain_sum + swapped(gain_sum, "narrow", 1))[0]
+    quarter = scan_width // 2
+    out_weight_grad = jnp.concatenate(
+        [x for total in sums for x in (total[:quarter], total[2 * quarter : 3 * quarter])]
+    ).astype(f32)
     return (
         layer_out,
         tokens_grad,
         norm_gain_grad,
-        joined(inner_weight_grad, gate_weight_grad),
+        joined(*sums, inner_sum),
         conv_sum[columns : columns + taps],
         conv_sum[columns + taps],
         conv_sum[:columns],
@@ -822,7 +940,7 @@
         scan_sum[rank + count + 1],
         scan_sum[rank : rank + count],
         scan_sum[rank + count],
-        out_weight_grad.astype(f32),
+        out_weight_grad,
     )
 
 

time: 302 us -> 291 us (0.964)
  waiting for transfers between devices: 141 us -> 105 us
  Pallas kernels: 52.7 us -> 63.4 us
  other arithmetic: 25.8 us -> 32 us
  matrix products: 12.1 us -> 17.4 us
    ppermute x42 -> x37, waiting for transfers between devices: 138 us -> 104 us  [swapped(): return lax.ppermute(array, axis, [(i, i ^ bit) for i in range(peers)])]
    ppermute x42 -> x37, starting transfers between devices: 48.4 us -> 37.7 us  [swapped(): return lax.ppermute(array, axis, [(i, i ^ bit) for i in range(peers)])]
    pallas_call x4 -> x7, Pallas kernels: 46.3 us -> 54.3 us  [call(): pl.pallas_call(kernel, grid=(width // scan_width,), in_specs=in_specs, ou...]
    ppermute x4 -> x6, starting transfers between devices: 9.65 us -> 17.2 us  [passed_along(): return lax.ppermute(array, axis, pairs)]
    ppermute x0 -> x1, starting transfers between devices: none -> 4.3 us  [to_next_both(): lax.ppermute(array, ('wide', 'narrow'), pairs)]
    add x10 -> x11, other arithmetic: 1.12 us -> 5.22 us  [the longest x3 2.34 us: first_step(): return jnp.concatenate(mine) + swapped(away, 'wide', 1).astype(f32)]
    pallas_call x1 -> x2, Pallas kernels: 6.42 us -> 9.12 us  [the longest x1 6.92 us: joined(): pl.pallas_call(join_kernel, grid=(4,), in_specs=[spec, spec, whole_spec(*...]
  transfers between devices with their start and end apart: 46 -> 44, of which waited for: 32 -> 20; matrix products, arithmetic and copies ran while one was open for 8% -> 14% of each run, Pallas kernels for 0% -> 14%
where the time goes in v3:
time: 291 us; the launch traced here: 290 us
  waiting for transfers between devices  105 us (36%)
  Pallas kernels  63.4 us (22%)
  starting transfers between devices  59.2 us (20%)
  other arithmetic  32 us (11%)
  matrix products  17.4 us (6%)
  local copies, waits for them, and re-layouts  11.1 us (4%)
    ppermute x37, waiting for transfers between devices, swapped(): return lax.ppermute(array, axis, [(i, i ^ bit) for i in range(peers)])  104 us
    pallas_call x7, Pallas kernels, call(): pl.pallas_call(kernel, grid=(width // scan_width,), in_specs=in_specs, ou...  54.3 us
    ppermute x37, starting transfers between devices, swapped(): return lax.ppermute(array, axis, [(i, i ^ bit) for i in range(peers)])  37.7 us
    ppermute x6, starting transfers between devices, passed_along(): return lax.ppermute(array, axis, pairs)  17.2 us
    pallas_call x1, Pallas kernels, joined(): pl.pallas_call(join_kernel, grid=(4,), in_specs=[spec, spec, whole_spec(*...  6.92 us
    dot_general x12, matrix products, times(): lax.dot_general(left, right, contract_first, preferred_element_type=f32)  5.89 us
  transfers between devices with their start and end apart: 44, of which 20 were waited for; matrix products, arithmetic and copies ran while one was open for 14% of the time, Pallas kernels for 14%

profile of v3, /device:TPU:0, one launch (start us, length us, event | category | flops | bytes accessed | tf_op | source)
XLA Modules:
  0.0 289.6 jit_solution(4672548771357526399)
XLA Ops:
  0.7 1.4 fusion.87
  2.1 1.4 slice_compare_fusion
  4.3 4.3 %collective-permute-start.2 = (bf16[16,512]{1,0:T(8,128)(2,1)S(1)}, bf16[16,512]{1,0:T(8,128)(2,1)S(1)}, u32[]{:S(2)}, u32[]{:S(2)}) collective-permute-start(bf16[16,512]{1,0:T(8,128)(2,1)S(1)} %slice_select_fusion.2), channel_id=1, source_target_pairs={{0,3},{1,2},{2,5},{3,4},{4,7},{5,6},{6,9},{7,8},{8,11},{9,10},{10,... | collective-permute-start | bytes 49160 | tf_op jit(solution)/shard_map/ppermute | solution.py:50
  8.6 3.5 %collective-permute-start.1 = (bf16[16,512]{1,0:T(8,128)(2,1)S(1)}, bf16[16,512]{1,0:T(8,128)(2,1)S(1)}, u32[]{:S(2)}, u32[]{:S(2)}) collective-permute-start(bf16[16,512]{1,0:T(8,128)(2,1)S(1)} %slice_select_fusion.2), channel_id=1, source_target_pairs={{0,2},{2,4},{4,6},{6,8},{8,10},{10,12},{12,14},{14,16},{16,18},{18... | collective-permute-start | bytes 49160 | tf_op jit(solution)/shard_map/ppermute | solution.py:27
  12.7 1.5 collective-permute-start.4
  15.8 1.5 compare_convert_fusion
  18.4 3.2 %collective-permute-done.other_ref = bf16[256,512]{1,0:T(8,128)(2,1)S(1)} collective-permute-done((bf16[256,512]{1,0:T(8,128)(2,1)}, bf16[256,512]{1,0:T(8,128)(2,1)S(1)}, u32[]{:S(2)}, u32[]{:S(2)}) %collective-permute-start) | collective-permute-done | bytes 262176 | tf_op jit(solution)/shard_map/ppermute | solution.py:32
  22.2 2.2 normalized.1
  24.4 4.9 %fusion.7.inner_ref.gate_ref = bf16[2,272,1024]{2,1,0:T(8,128)(2,1)} fusion(bf16[1024,2,1024]{2,1,0:T(2,128)(2,1)} %param.15, bf16[272,1024]{1,0:T(8,128)(2,1)} %get-tuple-element.40), kind=kOutput, calls=%fused_computation.12 | convolution fusion | flops 1141407744 | bytes 5865472 | tf_op jit(solution)/shard_map/td,dce->cte/dot_general | solution.py:795
  29.4 3.5 %convolve.1 = (f32[256,1024]{1,0:T(8,128)}, bf16[256,1024]{1,0:T(8,128)(2,1)}, f32[96,256]{1,0:T(8,128)}) custom-call(bf16[2,272,1024]{2,1,0:T(8,128)(2,1)} %fusion.7.inner_ref.gate_ref, f32[4,1024]{1,0:T(4,128)} %conv_weight_ref.5, f32[1,1024]{1,0:T(1,128)} %bitcast.81, bf16[96,1024]{1,0:T(8,128)(2,1)} %select_ref.5, f32[256,8]{1,0:T(8,128)} %copy.57.mask_ref), custom_call_target="tpu_custom_call" | custom-call | flops 4000000000 | bytes 1339392 | tf_op jit(solution)/shard_map/convolve/pallas_call | solution.py:134
  33.5 1.7 fusion.75.gated_grad_ref
  35.3 2.5 collective-permute-done.3.other_ref
  38.4 6.6 %scan_ends.2 = (f32[256,512]{1,0:T(8,128)}, f32[256,512]{1,0:T(8,128)}, f32[40,512]{1,0:T(8,128)}) custom-call(f32[96,256]{1,0:T(8,128)} %get-tuple-element.41.selected_ref, f32[96,256]{1,0:T(8,128)} %copy-done.27, bf16[64,1024]{1,0:T(8,128)(2,1)} %step_weight_ref.7, f32[1,1024]{1,0:T(1,128)} %bitcast.82, bf16[256,1024]{1,0:T(8,128)(2,1)} %get-tuple-element.42.act_ref, ...), custom_call_target="tpu_custom_call" | custom-call | flops 5000000000 | bytes 3092480 | tf_op jit(solution)/shard_map/scan_ends/pallas_call | solution.py:134
  45.1 6.7 %scan_ends.3 = (f32[256,512]{1,0:T(8,128)}, f32[256,512]{1,0:T(8,128)}, f32[40,512]{1,0:T(8,128)}) custom-call(f32[96,256]{1,0:T(8,128)} %get-tuple-element.41.selected_ref, f32[96,256]{1,0:T(8,128)} %copy-done.27, bf16[64,1024]{1,0:T(8,128)(2,1)} %step_weight_ref.7, f32[1,1024]{1,0:T(1,128)} %bitcast.83, bf16[256,1024]{1,0:T(8,128)(2,1)} %get-tuple-element.42.act_ref, ...), custom_call_target="tpu_custom_call" | custom-call | flops 5000000000 | bytes 3092480 | tf_op jit(solution)/shard_map/scan_ends/pallas_call | solution.py:134
  52.3 1.6 collective-permute-start.6
  54.0 2.7 collective-permute-done.6
  58.3 1.3 collective-permute-start.8
  59.6 4.7 %collective-permute-start.7 = (f32[16,512]{1,0:T(8,128)S(1)}, f32[16,512]{1,0:T(8,128)S(1)}, u32[]{:S(2)}, u32[]{:S(2)}) collective-permute-start(f32[16,512]{1,0:T(8,128)S(1)} %get-tuple-element.147), channel_id=1, source_target_pairs={{0,8},{2,10},{4,12},{6,14},{8,16},{10,18},{12,20},{14,22},{16,24},... | collective-permute-start | bytes 98312 | tf_op jit(solution)/shard_map/ppermute | solution.py:27
  64.4 1.6 collective-permute-start.10
  67.3 15.4 %scan_full.2 = (bf16[256,512]{1,0:T(8,128)(2,1)}, bf16[256,512]{1,0:T(8,128)(2,1)}, f32[256,512]{1,0:T(8,128)}, f32[96,256]{1,0:T(8,128)}, f32[96,512]{1,0:T(8,128)}) custom-call(f32[96,256]{1,0:T(8,128)} %get-tuple-element.41.selected_ref, f32[96,256]{1,0:T(8,128)} %copy-done.27, f32[256,512]{1,0:T(8,128)} %get-tuple-element.43.step_pre_ref, ...), custom_call_target="tpu_custom_call" | custom-call | flops 12999999488 | bytes 4403200 | tf_op jit(solution)/shard_map/scan_full/pallas_call | solution.py:134
  82.7 1.3 convolution_convert_fusion.5
  85.1 1.3 collective-permute-start.12
  86.4 4.8 %collective-permute-start.11 = (f32[16,512]{1,0:T(8,128)S(1)}, f32[16,512]{1,0:T(8,128)S(1)}, u32[]{:S(2)}, u32[]{:S(2)}) collective-permute-start(f32[16,512]{1,0:T(8,128)S(1)} %get-tuple-element.149), channel_id=1, source_target_pairs={{0,8},{2,10},{4,12},{6,14},{8,16},{10,18},{12,20},{14,22},{16,24},... | collective-permute-start | bytes 98312 | tf_op jit(solution)/shard_map/ppermute | solution.py:27
  93.3 1.7 maximum_add_fusion.after_ref
  94.9 15.5 %scan_full.3 = (bf16[256,512]{1,0:T(8,128)(2,1)}, bf16[256,512]{1,0:T(8,128)(2,1)}, f32[256,512]{1,0:T(8,128)}, f32[96,256]{1,0:T(8,128)}, f32[96,512]{1,0:T(8,128)}) custom-call(f32[96,256]{1,0:T(8,128)} %get-tuple-element.41.selected_ref, f32[96,256]{1,0:T(8,128)} %copy-done.27, f32[256,512]{1,0:T(8,128)} %get-tuple-element.47.step_pre_ref, ...), custom_call_target="tpu_custom_call" | custom-call | flops 12999999488 | bytes 6402048 | tf_op jit(solution)/shard_map/scan_full/pallas_call | solution.py:134
  110.4 1.2 fusion.51
  111.6 1.8 fusion.29
  116.6 1.6 collective-permute-start.29
  118.2 1.5 collective-permute-start.14
  122.0 3.3 %convolve_grad.2 = (bf16[256,512]{1,0:T(8,128)(2,1)}, f32[16,512]{1,0:T(8,128)}, f32[112,512]{1,0:T(8,128)}) custom-call(f32[96,256]{1,0:T(8,128)} %get-tuple-element.54.select_grad_ref, f32[96,256]{1,0:T(8,128)} %copy-done.29, bf16[96,1024]{1,0:T(8,128)(2,1)} %select_ref.5, f32[256,512]{1,0:T(8,128)} %get-tuple-element.55.act_grad_ref, ...), custom_call_target="tpu_custom_call" | custom-call | flops 3000000000 | bytes 3629056 | tf_op jit(solution)/shard_map/convolve_grad/pallas_call | solution.py:134
  126.1 3.3 %convolve_grad.3 = (bf16[256,512]{1,0:T(8,128)(2,1)}, f32[16,512]{1,0:T(8,128)}, f32[112,512]{1,0:T(8,128)}) custom-call(f32[96,256]{1,0:T(8,128)} %get-tuple-element.54.select_grad_ref, f32[96,256]{1,0:T(8,128)} %copy-done.29, bf16[96,1024]{1,0:T(8,128)(2,1)} %select_ref.5, f32[256,512]{1,0:T(8,128)} %get-tuple-element.58.act_grad_ref, ...), custom_call_target="tpu_custom_call" | custom-call | flops 3000000000 | bytes 3629056 | tf_op jit(solution)/shard_map/convolve_grad/pallas_call | solution.py:134
  130.2 1.5 collective-permute-start.16
  135.7 3.0 %fusion.15 = (f32[1024]{0:T(1024)S(1)}, f32[256]{0:T(256)S(1)}, f32[256,1024]{1,0:T(8,128)S(1)}) fusion(f32[256]{0:T(256)S(1)} %get-tuple-element.70, bf16[272,1024]{1,0:T(8,128)(2,1)} %get-tuple-element.63, f32[1024]{0:T(1024)S(1)} %copy-done.23, bf16[1024,2,1024]{2,1,0:T(2,128)(2,1)S(1)} %copy-done.26, bf16[1,256,1024]{2,1,0:T(8,128)(2,1)S(1)} %copy-done.12, ...), kind=kOutput, calls=%fused_computation.30 | convolution fusion | flops 1076099840 | bytes 6825984 | tf_op jit(solution)/shard_map/cte,dce->td/dot_general | solution.py:892
  139.3 2.2 collective-permute-start.20
  142.2 1.3 convert_add_fusion.2
  143.6 2.5 collective-permute-start.30
  146.2 6.4 %collective-permute-done.30 = bf16[128,1024]{1,0:T(8,128)(2,1)S(1)} collective-permute-done((bf16[128,1024]{1,0:T(8,128)(2,1)S(1)}, bf16[128,1024]{1,0:T(8,128)(2,1)S(1)}, u32[]{:S(2)}, u32[]{:S(2)}) %collective-permute-start.30) | collective-permute-done | bytes 262176 | tf_op jit(solution)/shard_map/ppermute | solution.py:32
  152.6 1.6 collective-permute-start.17
  154.4 3.2 %collective-permute-start.31 = (bf16[64,1024]{1,0:T(8,128)(2,1)S(1)}, bf16[64,1024]{1,0:T(8,128)(2,1)S(1)}, u32[]{:S(2)}, u32[]{:S(2)}) collective-permute-start(bf16[64,1024]{1,0:T(8,128)(2,1)S(1)} %select_convert_fusion.8), channel_id=1, source_target_pairs={{0,16},{2,18},{4,20},{6,22},{8,24},{10,26},{12,28},{14,30},{16,0},... | collective-permute-start | bytes 393224 | tf_op jit(solution)/shard_map/ppermute | solution.py:32
  157.6 5.4 %collective-permute-done.31 = bf16[64,1024]{1,0:T(8,128)(2,1)S(1)} collective-permute-done((bf16[64,1024]{1,0:T(8,128)(2,1)S(1)}, bf16[64,1024]{1,0:T(8,128)(2,1)S(1)}, u32[]{:S(2)}, u32[]{:S(2)}) %collective-permute-start.31) | collective-permute-done | bytes 131104 | tf_op jit(solution)/shard_map/ppermute | solution.py:32
  163.8 9.0 %collective-permute-done.32 = bf16[64,1024]{1,0:T(8,128)(2,1)S(1)} collective-permute-done((bf16[64,1024]{1,0:T(8,128)(2,1)S(1)}, bf16[64,1024]{1,0:T(8,128)(2,1)S(1)}, u32[]{:S(2)}, u32[]{:S(2)}) %collective-permute-start.32) | collective-permute-done | bytes 131104 | tf_op jit(solution)/shard_map/ppermute | solution.py:32
  173.3 1.7 collective-permute-start.37
  176.1 4.7 %collective-permute-done.33 = bf16[128,1024]{1,0:T(8,128)(2,1)S(1)} collective-permute-done((bf16[128,1024]{1,0:T(8,128)(2,1)S(1)}, bf16[128,1024]{1,0:T(8,128)(2,1)S(1)}, u32[]{:S(2)}, u32[]{:S(2)}) %collective-permute-start.33) | collective-permute-done | bytes 262176 | tf_op jit(solution)/shard_map/ppermute | solution.py:32
  180.9 1.7 collective-permute-start.34
  182.6 5.6 %collective-permute-done.37 = bf16[256,1024]{1,0:T(8,128)(2,1)S(1)} collective-permute-done((bf16[256,1024]{1,0:T(8,128)(2,1)S(1)}, bf16[256,1024]{1,0:T(8,128)(2,1)S(1)}, u32[]{:S(2)}, u32[]{:S(2)}) %collective-permute-start.37) | collective-permute-done | bytes 524320 | tf_op jit(solution)/shard_map/ppermute | solution.py:32
  188.5 2.1 collective-permute-start.38
  190.6 11.7 %collective-permute-done.21 = bf16[320,1024]{1,0:T(8,128)(2,1)S(1)} collective-permute-done((bf16[320,1024]{1,0:T(8,128)(2,1)S(1)}, bf16[320,1024]{1,0:T(8,128)(2,1)S(1)}, u32[]{:S(2)}, u32[]{:S(2)}) %collective-permute-start.21) | collective-permute-done | bytes 655392 | tf_op jit(solution)/shard_map/ppermute | solution.py:32
  202.7 2.1 collective-permute-start.22
  205.0 7.7 %collective-permute-done.22 = bf16[160,1024]{1,0:T(8,128)(2,1)S(1)} collective-permute-done((bf16[160,1024]{1,0:T(8,128)(2,1)S(1)}, bf16[160,1024]{1,0:T(8,128)(2,1)S(1)}, u32[]{:S(2)}, u32[]{:S(2)}) %collective-permute-start.22) | collective-permute-done | bytes 327712 | tf_op jit(solution)/shard_map/ppermute | solution.py:32
  214.0 3.2 %collective-permute-start.40 = (bf16[64,1024]{1,0:T(8,128)(2,1)S(1)}, bf16[64,1024]{1,0:T(8,128)(2,1)S(1)}, u32[]{:S(2)}, u32[]{:S(2)}) collective-permute-start(bf16[64,1024]{1,0:T(8,128)(2,1)S(1)} %add_convert_fusion.1), channel_id=1, source_target_pairs={{0,16},{2,18},{4,20},{6,22},{8,24},{10,26},{12,28},{14,30},{16,0},... | collective-permute-start | bytes 393224 | tf_op jit(solution)/shard_map/ppermute | solution.py:32
  217.1 7.2 %collective-permute-done.23 = bf16[80,1024]{1,0:T(8,128)(2,1)S(1)} collective-permute-done((bf16[80,1024]{1,0:T(8,128)(2,1)S(1)}, bf16[80,1024]{1,0:T(8,128)(2,1)S(1)}, u32[]{:S(2)}, u32[]{:S(2)}) %collective-permute-start.23) | collective-permute-done | bytes 163872 | tf_op jit(solution)/shard_map/ppermute | solution.py:32
  224.4 5.4 %collective-permute-done.40 = bf16[64,1024]{1,0:T(8,128)(2,1)S(1)} collective-permute-done((bf16[64,1024]{1,0:T(8,128)(2,1)S(1)}, bf16[64,1024]{1,0:T(8,128)(2,1)S(1)}, u32[]{:S(2)}, u32[]{:S(2)}) %collective-permute-start.40) | collective-permute-done | bytes 131104 | tf_op jit(solution)/shard_map/ppermute | solution.py:32
  230.0 4.0 %collective-permute-done.24 = bf16[80,1024]{1,0:T(8,128)(2,1)S(1)} collective-permute-done((bf16[80,1024]{1,0:T(8,128)(2,1)S(1)}, bf16[80,1024]{1,0:T(8,128)(2,1)S(1)}, u32[]{:S(2)}, u32[]{:S(2)}) %collective-permute-start.24) | collective-permute-done | bytes 163872 | tf_op jit(solution)/shard_map/ppermute | solution.py:32
  234.1 5.5 %collective-permute-done.41 = bf16[128,1024]{1,0:T(8,128)(2,1)S(1)} collective-permute-done((bf16[128,1024]{1,0:T(8,128)(2,1)S(1)}, bf16[128,1024]{1,0:T(8,128)(2,1)S(1)}, u32[]{:S(2)}, u32[]{:S(2)}) %collective-permute-start.41) | collective-permute-done | bytes 262176 | tf_op jit(solution)/shard_map/ppermute | solution.py:32
  241.0 4.7 %collective-permute-done.25 = bf16[160,1024]{1,0:T(8,128)(2,1)S(1)} collective-permute-done((bf16[160,1024]{1,0:T(8,128)(2,1)S(1)}, bf16[160,1024]{1,0:T(8,128)(2,1)S(1)}, u32[]{:S(2)}, u32[]{:S(2)}) %collective-permute-start.25) | collective-permute-done | bytes 327712 | tf_op jit(solution)/shard_map/ppermute | solution.py:32
  245.8 1.5 collective-permute-start.26
  247.8 7.0 %collective-permute-done.42 = bf16[256,1024]{1,0:T(8,128)(2,1)S(1)} collective-permute-done((bf16[256,1024]{1,0:T(8,128)(2,1)S(1)}, bf16[256,1024]{1,0:T(8,128)(2,1)S(1)}, u32[]{:S(2)}, u32[]{:S(2)}) %collective-permute-start.42) | collective-permute-done | bytes 524320 | tf_op jit(solution)/shard_map/ppermute | solution.py:32
  255.2 10.8 %collective-permute-done.26 = bf16[320,1024]{1,0:T(8,128)(2,1)S(1)} collective-permute-done((bf16[320,1024]{1,0:T(8,128)(2,1)S(1)}, bf16[320,1024]{1,0:T(8,128)(2,1)S(1)}, u32[]{:S(2)}, u32[]{:S(2)}) %collective-permute-start.26) | collective-permute-done | bytes 655392 | tf_op jit(solution)/shard_map/ppermute | solution.py:32
  266.5 2.1 fusion.26
  269.2 1.5 pad_maximum_fusion.1.first_ref
  271.3 1.5 pad_maximum_fusion.2.second_ref
  272.9 2.5 maximum_convert_fusion
  276.5 1.7 pad_maximum_fusion.inner_ref
  282.0 6.9 %joined.1 = f32[1024,2,1024]{2,1,0:T(2,128)} custom-call(bf16[1024,1024]{1,0:T(8,128)(2,1)} %pad_maximum_fusion.1.first_ref, bf16[1024,1024]{1,0:T(8,128)(2,1)} %pad_maximum_fusion.2.second_ref, bf16[1280,1024]{1,0:T(8,128)(2,1)} %pad_maximum_fusion.inner_ref), custom_call_target="tpu_custom_call" | custom-call | tf_op jit(solution)/shard_map/joined/pallas_call | solution.py:702
  (221 shorter events, 39.3 us)
Async XLA Ops:
  0.6 32.9 %copy-start = (bf16[1024,1024]{1,0:T(8,128)(2,1)S(1)}, bf16[1024,1024]{1,0:T(8,128)(2,1)}, u32[]{:S(2)}) copy-start(bf16[1024,1024]{1,0:T(8,128)(2,1)} %param.23) | copy-start | bytes 6291460
  4.3 14.1 %collective-permute-start.2 = (bf16[16,512]{1,0:T(8,128)(2,1)S(1)}, bf16[16,512]{1,0:T(8,128)(2,1)S(1)}, u32[]{:S(2)}, u32[]{:S(2)}) collective-permute-start(bf16[16,512]{1,0:T(8,128)(2,1)S(1)} %slice_select_fusion.2), channel_id=1, source_target_pairs={{0,3},{1,2},{2,5},{3,4},{4,7},{5,6},{6,9},{7,8},{8,11},{9,10},{10,... | collective-permute-start | bytes 49160 | tf_op jit(solution)/shard_map/ppermute | solution.py:50
  8.6 9.8 %collective-permute-start.1 = (bf16[16,512]{1,0:T(8,128)(2,1)S(1)}, bf16[16,512]{1,0:T(8,128)(2,1)S(1)}, u32[]{:S(2)}, u32[]{:S(2)}) collective-permute-start(bf16[16,512]{1,0:T(8,128)(2,1)S(1)} %slice_select_fusion.2), channel_id=1, source_target_pairs={{0,2},{2,4},{4,6},{6,8},{8,10},{10,12},{12,14},{14,16},{16,18},{18... | collective-permute-start | bytes 49160 | tf_op jit(solution)/shard_map/ppermute | solution.py:27
  12.1 9.4 %collective-permute-start = (bf16[256,512]{1,0:T(8,128)(2,1)}, bf16[256,512]{1,0:T(8,128)(2,1)S(1)}, u32[]{:S(2)}, u32[]{:S(2)}) collective-permute-start(bf16[256,512]{1,0:T(8,128)(2,1)} %own_ref.1), channel_id=1, source_target_pairs={{0,1},{1,0},{2,3},{3,2},{4,5},{5,4},{6,7},{7,6},{8,9},{9,8},{10,11... | collective-permute-start | bytes 786440 | tf_op jit(solution)/shard_map/ppermute | solution.py:32
  12.7 20.8 %collective-permute-start.4 = (bf16[256,512]{1,0:T(8,128)(2,1)}, bf16[256,512]{1,0:T(8,128)(2,1)S(1)}, u32[]{:S(2)}, u32[]{:S(2)}) collective-permute-start(bf16[256,512]{1,0:T(8,128)(2,1)} %param.25), channel_id=1, source_target_pairs={{0,1},{1,0},{2,3},{3,2},{4,5},{5,4},{6,7},{7,6},{8,9},{9,8},{10,11... | collective-permute-start | bytes 786440 | tf_op jit(solution)/shard_map/ppermute | solution.py:32
  18.3 3.2 %copy-start.24 = (bf16[16,512]{1,0:T(8,128)(2,1)}, bf16[16,512]{1,0:T(8,128)(2,1)S(1)}, u32[]{:S(2)}) copy-start(bf16[16,512]{1,0:T(8,128)(2,1)S(1)} %collective-permute-done.2.other_edge_ref) | copy-start | bytes 49156
  18.4 3.2 %copy-start.25 = (bf16[16,512]{1,0:T(8,128)(2,1)}, bf16[16,512]{1,0:T(8,128)(2,1)S(1)}, u32[]{:S(2)}) copy-start(bf16[16,512]{1,0:T(8,128)(2,1)S(1)} %collective-permute-done.1.edge_ref) | copy-start | bytes 49156
  29.4 4.1 %copy-start.8 = (bf16[256,512]{1,0:T(8,128)(2,1)S(1)}, bf16[256,512]{1,0:T(8,128)(2,1)}, u32[]{:S(2)}) copy-start(bf16[256,512]{1,0:T(8,128)(2,1)} %param.25) | copy-start | bytes 786436
  32.9 4.9 %collective-permute-start.3 = (f32[96,256]{1,0:T(8,128)}, f32[96,256]{1,0:T(8,128)S(1)}, u32[]{:S(2)}, u32[]{:S(2)}) collective-permute-start(f32[96,256]{1,0:T(8,128)} %get-tuple-element.41.selected_ref), channel_id=1, source_target_pairs={{0,1},{1,0},{2,3},{3,2},{4,5},{5,4},{6,7},{7,6},{8,9},{9,8},{10,11... | collective-permute-start | bytes 294920 | tf_op jit(solution)/shard_map/ppermute | solution.py:32
  45.0 7.2 %copy-start.22 = (f32[40,512]{1,0:T(8,128)S(1)}, f32[40,512]{1,0:T(8,128)}, u32[]{:S(2)}) copy-start(f32[40,512]{1,0:T(8,128)} %get-tuple-element.45) | copy-start | bytes 245764
  45.0 8.9 %copy-start.21 = (f32[256,1]{1,0:T(8,128)S(1)}, f32[256,1]{1,0:T(8,128)}, u32[]{:S(2)}) copy-start(f32[256,1]{1,0:T(8,128)} %get-tuple-element.53) | copy-start | bytes 3076
  45.0 7.2 %collective-permute-start.5 = (f32[40,512]{1,0:T(8,128)}, f32[40,512]{1,0:T(8,128)S(1)}, u32[]{:S(2)}, u32[]{:S(2)}) collective-permute-start(f32[40,512]{1,0:T(8,128)} %get-tuple-element.45), channel_id=1, source_target_pairs={{0,2},{2,0},{4,6},{6,4},{8,10},{10,8},{12,14},{14,12},{16,18},{18,... | collective-permute-start | bytes 245768 | tf_op jit(solution)/shard_map/ppermute | solution.py:32
  51.7 2.3 collective-permute-start.9
  52.3 4.5 %collective-permute-start.6 = (f32[40,512]{1,0:T(8,128)S(1)}, f32[40,512]{1,0:T(8,128)S(1)}, u32[]{:S(2)}, u32[]{:S(2)}) collective-permute-start(f32[40,512]{1,0:T(8,128)S(1)} %pad_maximum_fusion.14), channel_id=1, source_target_pairs={{0,4},{2,6},{4,0},{6,2},{8,12},{10,14},{12,8},{14,10},{16,20},{18,... | collective-permute-start | bytes 245768 | tf_op jit(solution)/shard_map/ppermute | solution.py:32
  58.3 7.7 %collective-permute-start.8 = (f32[16,512]{1,0:T(8,128)S(1)}, f32[16,512]{1,0:T(8,128)S(1)}, u32[]{:S(2)}, u32[]{:S(2)}) collective-permute-start(f32[16,512]{1,0:T(8,128)S(1)} %get-tuple-element.146), channel_id=1, source_target_pairs={{8,0},{10,2},{12,4},{14,6},{16,8},{18,10},{20,12},{22,14},{24,16},... | collective-permute-start | bytes 98312 | tf_op jit(solution)/shard_map/ppermute | solution.py:27
  59.6 6.4 %collective-permute-start.7 = (f32[16,512]{1,0:T(8,128)S(1)}, f32[16,512]{1,0:T(8,128)S(1)}, u32[]{:S(2)}, u32[]{:S(2)}) collective-permute-start(f32[16,512]{1,0:T(8,128)S(1)} %get-tuple-element.147), channel_id=1, source_target_pairs={{0,8},{2,10},{4,12},{6,14},{8,16},{10,18},{12,20},{14,22},{16,24},... | collective-permute-start | bytes 98312 | tf_op jit(solution)/shard_map/ppermute | solution.py:27
  64.4 20.7 %collective-permute-start.10 = (f32[40,512]{1,0:T(8,128)S(1)}, f32[40,512]{1,0:T(8,128)S(1)}, u32[]{:S(2)}, u32[]{:S(2)}) collective-permute-start(f32[40,512]{1,0:T(8,128)S(1)} %pad_maximum_fusion.15), channel_id=1, source_target_pairs={{0,4},{2,6},{4,0},{6,2},{8,12},{10,14},{12,8},{14,10},{16,20},{18,... | collective-permute-start | bytes 245768 | tf_op jit(solution)/shard_map/ppermute | solution.py:32
  84.9 8.4 %collective-permute-start.13 = (bf16[512,1024]{1,0:T(8,128)(2,1)S(1)}, bf16[512,1024]{1,0:T(8,128)(2,1)S(1)}, u32[]{:S(2)}, u32[]{:S(2)}) collective-permute-start(bf16[512,1024]{1,0:T(8,128)(2,1)S(1)} %maximum_maximum_fusion), channel_id=1, source_target_pairs={{0,2},{2,0},{4,6},{6,4},{8,10},{10,8},{12,14},{14,12},{16,18},{18,... | collective-permute-start | bytes 3145736 | tf_op jit(solution)/shard_map/ppermute | solution.py:32
  85.1 6.5 %collective-permute-start.12 = (f32[16,512]{1,0:T(8,128)S(1)}, f32[16,512]{1,0:T(8,128)S(1)}, u32[]{:S(2)}, u32[]{:S(2)}) collective-permute-start(f32[16,512]{1,0:T(8,128)S(1)} %get-tuple-element.148), channel_id=1, source_target_pairs={{8,0},{10,2},{12,4},{14,6},{16,8},{18,10},{20,12},{22,14},{24,16},... | collective-permute-start | bytes 98312 | tf_op jit(solution)/shard_map/ppermute | solution.py:27
  86.4 6.2 %collective-permute-start.11 = (f32[16,512]{1,0:T(8,128)S(1)}, f32[16,512]{1,0:T(8,128)S(1)}, u32[]{:S(2)}, u32[]{:S(2)}) collective-permute-start(f32[16,512]{1,0:T(8,128)S(1)} %get-tuple-element.149), channel_id=1, source_target_pairs={{0,8},{2,10},{4,12},{6,14},{8,16},{10,18},{12,20},{14,22},{16,24},... | collective-permute-start | bytes 98312 | tf_op jit(solution)/shard_map/ppermute | solution.py:27
  94.9 16.7 %copy-start.10 = (bf16[256,512]{1,0:T(8,128)(2,1)S(1)}, bf16[256,512]{1,0:T(8,128)(2,1)}, u32[]{:S(2)}) copy-start(bf16[256,512]{1,0:T(8,128)(2,1)} %get-tuple-element.46) | copy-start | bytes 786436
  111.6 3.0 %copy-start.2 = (f32[512,1024]{1,0:T(8,128)S(1)}, f32[512,1024]{1,0:T(8,128)}, u32[]{:S(2)}) copy-start(f32[512,1024]{1,0:T(8,128)} %maximum_add_fusion.after_ref) | copy-start | bytes 6291460
  115.9 4.9 %copy-start.11 = (bf16[256,512]{1,0:T(8,128)(2,1)S(1)}, bf16[256,512]{1,0:T(8,128)(2,1)}, u32[]{:S(2)}) copy-start(bf16[256,512]{1,0:T(8,128)(2,1)} %get-tuple-element.52) | copy-start | bytes 786436
  115.9 5.5 %collective-permute-start.15 = (f32[96,256]{1,0:T(8,128)S(1)}, f32[96,256]{1,0:T(8,128)S(1)}, u32[]{:S(2)}, u32[]{:S(2)}) collective-permute-start(f32[96,256]{1,0:T(8,128)S(1)} %copy-done.28), channel_id=1, source_target_pairs={{0,1},{1,0},{2,3},{3,2},{4,5},{5,4},{6,7},{7,6},{8,9},{9,8},{10,11... | collective-permute-start | bytes 294920 | tf_op jit(solution)/shard_map/ppermute | solution.py:32
  116.6 25.6 %collective-permute-start.29 = (bf16[256,1024]{1,0:T(8,128)(2,1)}, bf16[256,1024]{1,0:T(8,128)(2,1)}, u32[]{:S(2)}, u32[]{:S(2)}) collective-permute-start(bf16[256,1024]{1,0:T(8,128)(2,1)} %select_convert_fusion.2), channel_id=1, source_target_pairs={{0,4},{2,6},{4,0},{6,2},{8,12},{10,14},{12,8},{14,10},{16,20},{18,... | collective-permute-start | bytes 1572872 | tf_op jit(solution)/shard_map/ppermute | solution.py:32
  118.2 148.2 %collective-permute-start.14 = (f32[256,512]{1,0:T(8,128)S(1)}, f32[256,512]{1,0:T(8,128)}, u32[]{:S(2)}, u32[]{:S(2)}) collective-permute-start(f32[256,512]{1,0:T(8,128)S(1)} %slice_select_fusion.1), channel_id=1, source_target_pairs={{0,1},{1,0},{2,3},{3,2},{4,5},{5,4},{6,7},{7,6},{8,9},{9,8},{10,11... | collective-permute-start | bytes 1572872 | tf_op jit(solution)/shard_map/ppermute | solution.py:32
  129.4 4.0 %copy-start.15 = (bf16[256,512]{1,0:T(8,128)(2,1)S(1)}, bf16[256,512]{1,0:T(8,128)(2,1)}, u32[]{:S(2)}) copy-start(bf16[256,512]{1,0:T(8,128)(2,1)} %get-tuple-element.57) | copy-start | bytes 786436
  129.4 4.0 %copy-start.16 = (bf16[256,512]{1,0:T(8,128)(2,1)S(1)}, bf16[256,512]{1,0:T(8,128)(2,1)}, u32[]{:S(2)}) copy-start(bf16[256,512]{1,0:T(8,128)(2,1)} %get-tuple-element.59) | copy-start | bytes 786436
  130.2 3.1 %collective-permute-start.16 = (f32[8,1024]{1,0:T(8,128)S(1)}, f32[8,1024]{1,0:T(8,128)S(1)}, u32[]{:S(2)}, u32[]{:S(2)}) collective-permute-start(f32[8,1024]{1,0:T(8,128)S(1)} %slice.397), channel_id=1, source_target_pairs={{2,0},{4,2},{6,4},{8,6},{10,8},{12,10},{14,12},{16,14},{18,16},{20... | collective-permute-start | bytes 98312 | tf_op jit(solution)/shard_map/ppermute | solution.py:27
  131.8 41.0 %collective-permute-start.36 = (bf16[512,1024]{1,0:T(8,128)(2,1)S(1)}, bf16[512,1024]{1,0:T(8,128)(2,1)S(1)}, u32[]{:S(2)}, u32[]{:S(2)}) collective-permute-start(bf16[512,1024]{1,0:T(8,128)(2,1)S(1)} %maximum_maximum_fusion.3), channel_id=1, source_target_pairs={{0,2},{2,0},{4,6},{6,4},{8,10},{10,8},{12,14},{14,12},{16,18},{18,... | collective-permute-start | bytes 3145736 | tf_op jit(solution)/shard_map/ppermute | solution.py:32
  133.4 2.2 copy-start.12
  135.7 3.4 %copy-start.17 = (f32[112,512]{1,0:T(8,128)S(1)}, f32[112,512]{1,0:T(8,128)}, u32[]{:S(2)}) copy-start(f32[112,512]{1,0:T(8,128)} %get-tuple-element.66) | copy-start | bytes 688132
  135.7 3.4 %copy-start.18 = (f32[112,512]{1,0:T(8,128)S(1)}, f32[112,512]{1,0:T(8,128)}, u32[]{:S(2)}) copy-start(f32[112,512]{1,0:T(8,128)} %get-tuple-element.67) | copy-start | bytes 688132
  135.7 3.4 %copy-start.19 = (f32[96,512]{1,0:T(8,128)S(1)}, f32[96,512]{1,0:T(8,128)}, u32[]{:S(2)}) copy-start(f32[96,512]{1,0:T(8,128)} %get-tuple-element.64) | copy-start | bytes 589828
  135.7 3.4 %copy-start.20 = (f32[96,512]{1,0:T(8,128)S(1)}, f32[96,512]{1,0:T(8,128)}, u32[]{:S(2)}) copy-start(f32[96,512]{1,0:T(8,128)} %get-tuple-element.65) | copy-start | bytes 589828
  138.7 15.6 %collective-permute-start.18 = (f32[256,1]{0,1:T(1,128)S(1)}, f32[256,1]{0,1:T(1,128)S(1)}, u32[]{:S(2)}, u32[]{:S(2)}) collective-permute-start(f32[256,1]{0,1:T(1,128)S(1)} %bitcast.79), channel_id=1, source_target_pairs={{0,1},{1,0},{2,3},{3,2},{4,5},{5,4},{6,7},{7,6},{8,9},{9,8},{10,11... | collective-permute-start | bytes 3080 | tf_op jit(solution)/shard_map/ppermute | solution.py:32
  139.3 23.7 %collective-permute-start.20 = (bf16[128,1024]{1,0:T(8,128)(2,1)S(1)}, bf16[128,1024]{1,0:T(8,128)(2,1)S(1)}, u32[]{:S(2)}, u32[]{:S(2)}) collective-permute-start(bf16[128,1024]{1,0:T(8,128)(2,1)S(1)} %dynamic-slice_convert_fusion), channel_id=1, source_target_pairs={{0,2},{2,0},{4,6},{6,4},{8,10},{10,8},{12,14},{14,12},{16,18},{18,... | collective-permute-start | bytes 786440 | tf_op jit(solution)/shard_map/ppermute | solution.py:32
  143.6 9.0 %collective-permute-start.30 = (bf16[128,1024]{1,0:T(8,128)(2,1)S(1)}, bf16[128,1024]{1,0:T(8,128)(2,1)S(1)}, u32[]{:S(2)}, u32[]{:S(2)}) collective-permute-start(bf16[128,1024]{1,0:T(8,128)(2,1)S(1)} %select_convert_fusion.5), channel_id=1, source_target_pairs={{0,8},{2,10},{4,12},{6,14},{8,0},{10,2},{12,4},{14,6},{16,24},{18,... | collective-permute-start | bytes 786440 | tf_op jit(solution)/shard_map/ppermute | solution.py:32
  152.6 113.9 %collective-permute-start.17 = (f32[256,512]{1,0:T(8,128)S(1)}, f32[256,512]{1,0:T(8,128)S(1)}, u32[]{:S(2)}, u32[]{:S(2)}) collective-permute-start(f32[256,512]{1,0:T(8,128)S(1)} %slice_select_fusion), channel_id=1, source_target_pairs={{0,1},{1,0},{2,3},{3,2},{4,5},{5,4},{6,7},{7,6},{8,9},{9,8},{10,11... | collective-permute-start | bytes 1572872 | tf_op jit(solution)/shard_map/ppermute | solution.py:32
  154.3 18.6 %copy-start.5 = (f32[256,512]{1,0:T(8,128)S(1)}, f32[256,512]{1,0:T(8,128)}, u32[]{:S(2)}) copy-start(f32[256,512]{1,0:T(8,128)} %get-tuple-element.96) | copy-start | bytes 1572868
  154.3 18.6 %copy-start.6 = (f32[256,512]{1,0:T(8,128)S(1)}, f32[256,512]{1,0:T(8,128)}, u32[]{:S(2)}) copy-start(f32[256,512]{1,0:T(8,128)} %get-tuple-element.97) | copy-start | bytes 1572868
  154.4 8.6 %collective-permute-start.31 = (bf16[64,1024]{1,0:T(8,128)(2,1)S(1)}, bf16[64,1024]{1,0:T(8,128)(2,1)S(1)}, u32[]{:S(2)}, u32[]{:S(2)}) collective-permute-start(bf16[64,1024]{1,0:T(8,128)(2,1)S(1)} %select_convert_fusion.8), channel_id=1, source_target_pairs={{0,16},{2,18},{4,20},{6,22},{8,24},{10,26},{12,28},{14,30},{16,0},... | collective-permute-start | bytes 393224 | tf_op jit(solution)/shard_map/ppermute | solution.py:32
  163.0 12.0 %collective-permute-start.19 = (bf16[512,1024]{1,0:T(8,128)(2,1)S(1)}, bf16[512,1024]{1,0:T(8,128)(2,1)S(1)}, u32[]{:S(2)}, u32[]{:S(2)}) collective-permute-start(bf16[512,1024]{1,0:T(8,128)(2,1)S(1)} %maximum_maximum_fusion.1), channel_id=1, source_target_pairs={{0,2},{2,0},{4,6},{6,4},{8,10},{10,8},{12,14},{14,12},{16,18},{18,... | collective-permute-start | bytes 3145736 | tf_op jit(solution)/shard_map/ppermute | solution.py:32
  163.0 9.7 %collective-permute-start.32 = (bf16[64,1024]{1,0:T(8,128)(2,1)S(1)}, bf16[64,1024]{1,0:T(8,128)(2,1)S(1)}, u32[]{:S(2)}, u32[]{:S(2)}) collective-permute-start(bf16[64,1024]{1,0:T(8,128)(2,1)S(1)} %add_convert_fusion.2), channel_id=1, source_target_pairs={{0,16},{2,18},{4,20},{6,22},{8,24},{10,26},{12,28},{14,30},{16,0},... | collective-permute-start | bytes 393224 | tf_op jit(solution)/shard_map/ppermute | solution.py:32
  172.8 8.0 %collective-permute-start.33 = (bf16[128,1024]{1,0:T(8,128)(2,1)S(1)}, bf16[128,1024]{1,0:T(8,128)(2,1)S(1)}, u32[]{:S(2)}, u32[]{:S(2)}) collective-permute-start(bf16[128,1024]{1,0:T(8,128)(2,1)S(1)} %pad_maximum_fusion.12), channel_id=1, source_target_pairs={{0,8},{2,10},{4,12},{6,14},{8,0},{10,2},{12,4},{14,6},{16,24},{18,... | collective-permute-start | bytes 786440 | tf_op jit(solution)/shard_map/ppermute | solution.py:32
  173.3 14.9 %collective-permute-start.37 = (bf16[256,1024]{1,0:T(8,128)(2,1)S(1)}, bf16[256,1024]{1,0:T(8,128)(2,1)S(1)}, u32[]{:S(2)}, u32[]{:S(2)}) collective-permute-start(bf16[256,1024]{1,0:T(8,128)(2,1)S(1)} %select_convert_fusion.1), channel_id=1, source_target_pairs={{0,4},{2,6},{4,0},{6,2},{8,12},{10,14},{12,8},{14,10},{16,20},{18,... | collective-permute-start | bytes 1572872 | tf_op jit(solution)/shard_map/ppermute | solution.py:32
  175.6 26.6 %collective-permute-start.21 = (bf16[320,1024]{1,0:T(8,128)(2,1)S(1)}, bf16[320,1024]{1,0:T(8,128)(2,1)S(1)}, u32[]{:S(2)}, u32[]{:S(2)}) collective-permute-start(bf16[320,1024]{1,0:T(8,128)(2,1)S(1)} %select_convert_fusion), channel_id=1, source_target_pairs={{0,4},{2,6},{4,0},{6,2},{8,12},{10,14},{12,8},{14,10},{16,20},{18,... | collective-permute-start | bytes 1966088 | tf_op jit(solution)/shard_map/ppermute | solution.py:32
  180.9 66.4 %collective-permute-start.34 = (bf16[256,1024]{1,0:T(8,128)(2,1)S(1)}, bf16[256,1024]{1,0:T(8,128)(2,1)S(1)}, u32[]{:S(2)}, u32[]{:S(2)}) collective-permute-start(bf16[256,1024]{1,0:T(8,128)(2,1)S(1)} %pad_maximum_fusion.9), channel_id=1, source_target_pairs={{0,4},{2,6},{4,0},{6,2},{8,12},{10,14},{12,8},{14,10},{16,20},{18,... | collective-permute-start | bytes 1572872 | tf_op jit(solution)/shard_map/ppermute | solution.py:32
  188.5 16.3 %collective-permute-start.38 = (bf16[128,1024]{1,0:T(8,128)(2,1)S(1)}, bf16[128,1024]{1,0:T(8,128)(2,1)S(1)}, u32[]{:S(2)}, u32[]{:S(2)}) collective-permute-start(bf16[128,1024]{1,0:T(8,128)(2,1)S(1)} %select_convert_fusion.4), channel_id=1, source_target_pairs={{0,8},{2,10},{4,12},{6,14},{8,0},{10,2},{12,4},{14,6},{16,24},{18,... | collective-permute-start | bytes 786440 | tf_op jit(solution)/shard_map/ppermute | solution.py:32
  202.7 10.1 %collective-permute-start.22 = (bf16[160,1024]{1,0:T(8,128)(2,1)S(1)}, bf16[160,1024]{1,0:T(8,128)(2,1)S(1)}, u32[]{:S(2)}, u32[]{:S(2)}) collective-permute-start(bf16[160,1024]{1,0:T(8,128)(2,1)S(1)} %select_convert_fusion.3), channel_id=1, source_target_pairs={{0,8},{2,10},{4,12},{6,14},{8,0},{10,2},{12,4},{14,6},{16,24},{18,... | collective-permute-start | bytes 983048 | tf_op jit(solution)/shard_map/ppermute | solution.py:32
  204.9 9.0 %collective-permute-start.39 = (bf16[64,1024]{1,0:T(8,128)(2,1)S(1)}, bf16[64,1024]{1,0:T(8,128)(2,1)S(1)}, u32[]{:S(2)}, u32[]{:S(2)}) collective-permute-start(bf16[64,1024]{1,0:T(8,128)(2,1)S(1)} %select_convert_fusion.7), channel_id=1, source_target_pairs={{0,16},{2,18},{4,20},{6,22},{8,24},{10,26},{12,28},{14,30},{16,0},... | collective-permute-start | bytes 393224 | tf_op jit(solution)/shard_map/ppermute | solution.py:32
  212.9 11.3 %collective-permute-start.23 = (bf16[80,1024]{1,0:T(8,128)(2,1)S(1)}, bf16[80,1024]{1,0:T(8,128)(2,1)S(1)}, u32[]{:S(2)}, u32[]{:S(2)}) collective-permute-start(bf16[80,1024]{1,0:T(8,128)(2,1)S(1)} %select_convert_fusion.6), channel_id=1, source_target_pairs={{0,16},{2,18},{4,20},{6,22},{8,24},{10,26},{12,28},{14,30},{16,0},... | collective-permute-start | bytes 491528 | tf_op jit(solution)/shard_map/ppermute | solution.py:32
  214.0 15.8 %collective-permute-start.40 = (bf16[64,1024]{1,0:T(8,128)(2,1)S(1)}, bf16[64,1024]{1,0:T(8,128)(2,1)S(1)}, u32[]{:S(2)}, u32[]{:S(2)}) collective-permute-start(bf16[64,1024]{1,0:T(8,128)(2,1)S(1)} %add_convert_fusion.1), channel_id=1, source_target_pairs={{0,16},{2,18},{4,20},{6,22},{8,24},{10,26},{12,28},{14,30},{16,0},... | collective-permute-start | bytes 393224 | tf_op jit(solution)/shard_map/ppermute | solution.py:32
  224.3 9.6 %collective-permute-start.24 = (bf16[80,1024]{1,0:T(8,128)(2,1)S(1)}, bf16[80,1024]{1,0:T(8,128)(2,1)S(1)}, u32[]{:S(2)}, u32[]{:S(2)}) collective-permute-start(bf16[80,1024]{1,0:T(8,128)(2,1)S(1)} %add_convert_fusion), channel_id=1, source_target_pairs={{0,16},{2,18},{4,20},{6,22},{8,24},{10,26},{12,28},{14,30},{16,0},... | collective-permute-start | bytes 491528 | tf_op jit(solution)/shard_map/ppermute | solution.py:32
  229.9 9.8 %collective-permute-start.41 = (bf16[128,1024]{1,0:T(8,128)(2,1)S(1)}, bf16[128,1024]{1,0:T(8,128)(2,1)S(1)}, u32[]{:S(2)}, u32[]{:S(2)}) collective-permute-start(bf16[128,1024]{1,0:T(8,128)(2,1)S(1)} %pad_maximum_fusion.13), channel_id=1, source_target_pairs={{0,8},{2,10},{4,12},{6,14},{8,0},{10,2},{12,4},{14,6},{16,24},{18,... | collective-permute-start | bytes 786440 | tf_op jit(solution)/shard_map/ppermute | solution.py:32
  234.0 11.6 %collective-permute-start.25 = (bf16[160,1024]{1,0:T(8,128)(2,1)S(1)}, bf16[160,1024]{1,0:T(8,128)(2,1)S(1)}, u32[]{:S(2)}, u32[]{:S(2)}) collective-permute-start(bf16[160,1024]{1,0:T(8,128)(2,1)S(1)} %pad_maximum_fusion.11), channel_id=1, source_target_pairs={{0,8},{2,10},{4,12},{6,14},{8,0},{10,2},{12,4},{14,6},{16,24},{18,... | collective-permute-start | bytes 983048 | tf_op jit(solution)/shard_map/ppermute | solution.py:32
  239.8 14.9 %collective-permute-start.42 = (bf16[256,1024]{1,0:T(8,128)(2,1)S(1)}, bf16[256,1024]{1,0:T(8,128)(2,1)S(1)}, u32[]{:S(2)}, u32[]{:S(2)}) collective-permute-start(bf16[256,1024]{1,0:T(8,128)(2,1)S(1)} %pad_maximum_fusion.10), channel_id=1, source_target_pairs={{0,4},{2,6},{4,0},{6,2},{8,12},{10,14},{12,8},{14,10},{16,20},{18,... | collective-permute-start | bytes 1572872 | tf_op jit(solution)/shard_map/ppermute | solution.py:32
  245.8 20.1 %collective-permute-start.26 = (bf16[320,1024]{1,0:T(8,128)(2,1)S(1)}, bf16[320,1024]{1,0:T(8,128)(2,1)S(1)}, u32[]{:S(2)}, u32[]{:S(2)}) collective-permute-start(bf16[320,1024]{1,0:T(8,128)(2,1)S(1)} %pad_maximum_fusion.7), channel_id=1, source_target_pairs={{0,4},{2,6},{4,0},{6,2},{8,12},{10,14},{12,8},{14,10},{16,20},{18,... | collective-permute-start | bytes 1966088 | tf_op jit(solution)/shard_map/ppermute | solution.py:32
  247.7 20.9 %collective-permute-start.35 = (bf16[512,1024]{1,0:T(8,128)(2,1)S(1)}, bf16[512,1024]{1,0:T(8,128)(2,1)S(1)}, u32[]{:S(2)}, u32[]{:S(2)}) collective-permute-start(bf16[512,1024]{1,0:T(8,128)(2,1)S(1)} %pad_maximum_fusion.5), channel_id=1, source_target_pairs={{0,2},{2,0},{4,6},{6,4},{8,10},{10,8},{12,14},{14,12},{16,18},{18,... | collective-permute-start | bytes 3145736 | tf_op jit(solution)/shard_map/ppermute | solution.py:32
  255.1 11.4 %copy-start.7 = (bf16[256,512]{1,0:T(8,128)(2,1)S(1)}, bf16[256,512]{1,0:T(8,128)(2,1)}, u32[]{:S(2)}) copy-start(bf16[256,512]{1,0:T(8,128)(2,1)} %own_ref.1) | copy-start | bytes 786436
  255.1 15.6 %collective-permute-start.43 = (bf16[512,1024]{1,0:T(8,128)(2,1)S(1)}, bf16[512,1024]{1,0:T(8,128)(2,1)S(1)}, u32[]{:S(2)}, u32[]{:S(2)}) collective-permute-start(bf16[512,1024]{1,0:T(8,128)(2,1)S(1)} %pad_maximum_fusion.6), channel_id=1, source_target_pairs={{0,2},{2,0},{4,6},{6,4},{8,10},{10,8},{12,14},{14,12},{16,18},{18,... | collective-permute-start | bytes 3145736 | tf_op jit(solution)/shard_map/ppermute | solution.py:32
  266.4 9.0 %collective-permute-start.27 = (bf16[640,1024]{1,0:T(8,128)(2,1)S(1)}, bf16[640,1024]{1,0:T(8,128)(2,1)S(1)}, u32[]{:S(2)}, u32[]{:S(2)}) collective-permute-start(bf16[640,1024]{1,0:T(8,128)(2,1)S(1)} %pad_maximum_fusion.4), channel_id=1, source_target_pairs={{0,2},{2,0},{4,6},{6,4},{8,10},{10,8},{12,14},{14,12},{16,18},{18,... | collective-permute-start | bytes 3932168 | tf_op jit(solution)/shard_map/ppermute | solution.py:32
  279.5 9.4 %collective-permute-start.28 = (f32[1,1024]{1,0:T(1,128)S(1)}, f32[1,1024]{1,0:T(1,128)S(1)}, u32[]{:S(2)}, u32[]{:S(2)}) collective-permute-start(f32[1,1024]{1,0:T(1,128)S(1)} %get-tuple-element.111), channel_id=1, source_target_pairs={{0,1},{1,0},{2,3},{3,2},{4,5},{5,4},{6,7},{7,6},{8,9},{9,8},{10,11... | collective-permute-start | bytes 12296 | tf_op jit(solution)/shard_map/ppermute | solution.py:32
  282.0 7.5 %copy-start.1 = (bf16[1024,1024]{1,0:T(8,128)(2,1)S(1)}, bf16[1024,1024]{1,0:T(8,128)(2,1)}, u32[]{:S(2)}) copy-start(bf16[1024,1024]{1,0:T(8,128)(2,1)} %param.23) | copy-start | bytes 6291460
  (10 other events, 14.7 us)

commit v4 on v3

--- a/solution.py
+++ b/solution.py
@@ -54,58 +54,67 @@
     return (lax.axis_index("wide") & bit) != 0
 
 
-def scatter_step(piece, bit):
-    half = piece.shape[0] // 2
-    low, high = piece[:half], piece[half:]
-    away = jnp.where(is_upper(bit), low, high).astype(bf16)
-    return jnp.where(is_upper(bit), high, low) + swapped(away, "wide", bit).astype(f32)
-
-
-def gather_step(held, bit):
-    other = swapped(held, "wide", bit)
-    upper = is_upper(bit)
-    return jnp.concatenate([jnp.where(upper, other, held), jnp.where(upper, held, other)])
+def group_bits(size):
+    bits, bit = [], 4
+    while bit < lax.axis_size("wide"):
+        bits.append(bit)
+        bit *= 2
+    return [tuple(bits[k : k + size]) for k in range(0, len(bits), size)]
+
+
+def flips(bits):
+    return [sum(b for k, b in enumerate(bits) if n >> k & 1) for n in range(2 ** len(bits))]
 
 
 def scattered(piece, bits):
+    rows = piece.shape[0] // 2 ** len(bits)
+    here = sum(is_upper(b).astype(jnp.int32) << k for k, b in enumerate(bits))
+
+    def block(n):
+        return lax.dynamic_slice_in_dim(piece, (here ^ n) * rows, rows, 0)
+
+    total = block(0).astype(f32)
+    for n, flip in enumerate(flips(bits)):
+        if n > 0:
+            total = total + swapped(block(n).astype(bf16), "wide", flip).astype(f32)
+    return total
+
+
+def gathered(held, bits):
+    blocks = [held] + [swapped(held, "wide", flip) for flip in flips(bits)[1:]]
     for bit in bits:
-        piece = scatter_step(piece, bit)
-    return piece.astype(bf16)
-
-
-def gathered(held, bits):
-    for bit in reversed(bits):
-        held = gather_step(held, bit)
+        upper = is_upper(bit)
+        blocks = [
+            jnp.concatenate([jnp.where(upper, b, a), jnp.where(upper, a, b)])
+            for a, b in zip(blocks[0::2], blocks[1::2])
+        ]
+    return blocks[0]
+
+
+def summed_above(piece, size):
+    for bits in group_bits(size):
+        piece = scattered(piece, bits)
+    held = piece.astype(bf16)
+    for bits in reversed(group_bits(size)):
+        held = gathered(held, bits)
     return held
 
 
-def halves_of(array, axis):
-    upper = lax.axis_index("wide") & 1
-    half = array.shape[axis] // 2
-    return (
-        lax.dynamic_slice_in_dim(array, upper * half, half, axis),
-        lax.dynamic_slice_in_dim(array, (1 - upper) * half, half, axis),
-    )
-
-
-def packed_rows(product):
-    half = product.shape[0] // 2
-    return jnp.concatenate([product[:half], product[half:]], axis=1)
-
-
-def times(left, right):
-    return lax.dot_general(left, right, contract_first, preferred_element_type=f32)
-
-
-def first_step(parts):
-    mine, send = [], []
-    for left, right, pack in parts:
-        own, other = halves_of(left, 1)
-        keep_product, send_product = times(own, right), times(other, right)
-        mine.append(packed_rows(keep_product) if pack else keep_product)
-        send.append(packed_rows(send_product) if pack else send_product)
-    away = jnp.concatenate(send).astype(bf16)
-    return jnp.concatenate(mine) + swapped(away, "wide", 1).astype(f32)
+def shared_by_four(array):
+    near = jnp.stack([array, swapped(array, "wide", 2)])
+    return near, swapped(near, "wide", 1)
+
+
+def quarter_of_four(array):
+    width = array.shape[1] // 4
+    here = lax.axis_index("wide") & 3
+
+    def quarter(n):
+        return lax.dynamic_slice_in_dim(array, (here ^ n) * width, width, 1)
+
+    return jnp.stack(
+        [quarter(0)] + [swapped(quarter(n), "wide", n) for n in (2, 1, 3)]
+    )
 
 
 def silu_slope(values):
@@ -364,25 +373,27 @@
     skip_ref,
     step_weight_ref,
     before_ref,
-    after_ref,
-    gated_ref,
-    gate_grad_ref,
-    act_grad_ref,
-    select_grad_ref,
-    small_ref,
-    coef,
-    held_step,
-    drive,
-    scan_grad,
-    scanned,
-    weighted,
-    states,
-    factors,
-    halves,
-    more_halves,
-    in_sum,
-    read_sum,
+    *rest,
+    waits,
 ):
+    (
+        pair_ref,
+        act_grad_ref,
+        select_grad_ref,
+        small_ref,
+        coef,
+        held_step,
+        drive,
+        scan_grad,
+        scanned,
+        weighted,
+        states,
+        factors,
+        halves,
+        more_halves,
+        in_sum,
+        read_sum,
+    ) = rest[waits:]
     rows = step_ref.shape[0]
     count = decay_log_ref.shape[0]
     rank = step_weight_ref.shape[0]
@@ -423,9 +434,9 @@
     grads = gated_grad * gate_act
     scan_grad[...] = grads
     total = scanned[...] + skip_ref[...] * act
-    gated_ref[...] = (total * gate_act).astype(bf16)
+    pair_ref[0] = (total * gate_act).astype(bf16)
     slope = logistic * (1.0 + gate * (1.0 - logistic))
-    gate_grad_ref[...] = (gated_grad * total * slope).astype(bf16)
+    pair_ref[1] = (gated_grad * total * slope).astype(bf16)
     small_ref[rank + count : rank + count + 1, :] = jnp.sum(grads * act, axis=0, keepdims=True)
 
     def backward(k, carried):
@@ -487,7 +498,7 @@
     skip_gain,
     step_weight,
     before,
-    after,
+    waits,
 ):
     rows, width = step.shape
     count = decay_log.shape[0]
@@ -496,7 +507,7 @@
     half_rows = 8 * body_rows * (scan_width // lanes)
     small = rank + count + 16
     return call(
-        scan_kernel,
+        functools.partial(scan_kernel, waits=len(waits)),
         "scan_full",
         width,
         [
@@ -514,12 +525,16 @@
             column_spec(1, part),
             column_spec(rank, part),
             whole_spec(columns, rows),
-            pl.BlockSpec(memory_space=pl.ANY),
+        ]
+        + [pl.BlockSpec(memory_space=pl.ANY)] * len(waits),
+        [
+            pl.BlockSpec((2, rows, scan_width), lambda j: (0, 0, j)),
+            column_spec(rows),
+            whole_spec(columns, rows),
+            column_spec(small),
         ],
-        [column_spec(rows)] * 3 + [whole_spec(columns, rows), column_spec(small)],
         [
-            jax.ShapeDtypeStruct((rows, width), bf16),
-            jax.ShapeDtypeStruct((rows, width), bf16),
+            jax.ShapeDtypeStruct((2, rows, width), bf16),
             jax.ShapeDtypeStruct((rows, width), f32),
             jax.ShapeDtypeStruct((columns, rows), f32),
             jax.ShapeDtypeStruct((small, width), f32),
@@ -549,7 +564,7 @@
         skip_gain,
         step_weight,
         before,
-        after,
+        *waits,
     )
 
 
@@ -678,36 +693,162 @@
     )(own, other, edge, other_edge, gain)
 
 
-def join_kernel(first_ref, second_ref, inner_ref, out_ref):
-    half = scan_width
-    step = pl.program_id(0)
-    rows = first_ref.shape[0]
-    core_rows = inner_ref.shape[0] // 2
-    out_ref[:, 1, :half] = first_ref[...].astype(f32)
-    out_ref[:, 1, half:] = second_ref[...].astype(f32)
-    for k in range(4):
-
-        @pl.when(step == k)
+def edge_kernel(ids_ref, tokens_ref, out_ref):
+    rows = ids_ref.shape[0]
+    taps = 4
+    out_ref[...] = tokens_ref[...]
+    place = lax.broadcasted_iota(jnp.int32, (halo, 1), 0)
+    same = jnp.zeros((halo, 1), f32)
+    for lag in range(taps):
+        here = jnp.where(ids_ref[rows - 1 - lag] == ids_ref[rows - 1], 1.0, 0.0)
+        same = same + jnp.where(place == halo - 1 - lag, here, 0.0)
+    out_ref[...] = (tokens_ref[...].astype(f32) * same).astype(bf16)
+
+
+def edge_rows_of(ids, tokens):
+    rows, width = tokens.shape
+    return pl.pallas_call(
+        edge_kernel,
+        grid=(1,),
+        in_specs=[
+            pl.BlockSpec(memory_space=pltpu.SMEM),
+            pl.BlockSpec((halo, width), lambda j: (rows // halo - 1, 0)),
+        ],
+        out_specs=pl.BlockSpec((halo, width), lambda j: (0, 0)),
+        out_shape=jax.ShapeDtypeStruct((halo, width), bf16),
+        name="edge_rows",
+    )(ids, tokens)
+
+
+def outer_kernel(near_ref, far_ref, normed_ref, cot_ref, out_ref):
+    quarter = cot_ref.shape[2]
+    out_sum, gate_sum = None, None
+    for n, pair in enumerate((near_ref[0], near_ref[1], far_ref[0], far_ref[1])):
+        first = lax.dot_general(pair[0], cot_ref[n], contract_first, preferred_element_type=f32)
+        second = lax.dot_general(normed_ref[n], pair[1], contract_first, preferred_element_type=f32)
+        out_sum = first if out_sum is None else out_sum + first
+        gate_sum = second if gate_sum is None else gate_sum + second
+    out_ref[:, :quarter] = out_sum[:quarter]
+    out_ref[:, quarter : 2 * quarter] = out_sum[quarter:]
+    out_ref[:, 2 * quarter :] = gate_sum
+
+
+def outer_quarters(near, far, normed, cot):
+    quarter = cot.shape[2]
+    return pl.pallas_call(
+        outer_kernel,
+        out_shape=jax.ShapeDtypeStruct((quarter, 4 * quarter), f32),
+        compiler_params=pltpu.CompilerParams(vmem_limit_bytes=vmem_bytes),
+        cost_estimate=pl.CostEstimate(
+            flops=2_000_000_000, bytes_accessed=4_000_000, transcendentals=0
+        ),
+        name="outer_quarters",
+    )(near, far, normed, cot)
+
+
+def select_block(step, place, refs, use):
+    flip = place ^ step
+    for core in range(2):
+
+        @pl.when((flip & 1) == core)
         def _():
-            at, lane = (k // 2) * core_rows, (k % 2) * half
-            for part in range(2):
-                block = inner_ref[at + part * rows : at + (part + 1) * rows, lane : lane + half]
-                out_ref[:, 0, part * half : (part + 1) * half] = block.astype(f32)
-
-
-def joined(first, second, inner):
-    depth = first.shape[0]
-    rows = depth // 4
-    spec = pl.BlockSpec((rows, scan_width), lambda j: (1 + 2 * (j // 2), j % 2))
+            use([ref[core] for ref in refs])
+
+
+def out_join_kernel(place_ref, first_near, first_far, second_near, second_far, out_ref):
+    quarter = out_ref.shape[1]
+
+    def use(blocks):
+        for part, block in enumerate(blocks):
+            for lane in range(2):
+                at = (2 * part + lane) * quarter
+                out_ref[at : at + quarter, :] = block[0, :, lane * quarter : (lane + 1) * quarter].astype(f32)
+
+    select_block(
+        pl.program_id(0), place_ref[0], [(first_near, first_far), (second_near, second_far)], use
+    )
+
+
+def in_join_kernel(
+    place_ref,
+    first_near,
+    first_far,
+    second_near,
+    second_far,
+    inner_near,
+    inner_far,
+    out_ref,
+    small_ref,
+    *,
+    groups,
+):
+    rows, half = out_ref.shape[0], out_ref.shape[2] // 2
+    piece = inner_near.shape[1] // groups
+    inner_rows = rows // groups
+    spare = piece - inner_rows
+
+    def use(blocks):
+        first, second, inner = blocks
+        out_ref[:, 1, :half] = first[0, :, half:].astype(f32)
+        out_ref[:, 1, half:] = second[0, :, half:].astype(f32)
+        for n in range(groups):
+            at = n * piece
+            block = inner[0, at : at + piece, :].astype(f32)
+            out_ref[n * inner_rows : (n + 1) * inner_rows, 0, :] = block[:inner_rows]
+            small_ref[n * spare : (n + 1) * spare, :] = block[inner_rows:]
+
+    select_block(
+        pl.program_id(0),
+        place_ref[0],
+        [(first_near, first_far), (second_near, second_far), (inner_near, inner_far)],
+        use,
+    )
+
+
+def from_four(array):
+    return pl.BlockSpec((1,) + array.shape[1:], lambda j, place: ((place[0] ^ j) // 2, 0, 0))
+
+
+def joined_out(place, first, second):
+    quarter = first[0].shape[1]
+    operands = [*first, *second]
     return pl.pallas_call(
-        join_kernel,
-        grid=(4,),
-        in_specs=[spec, spec, whole_spec(*inner.shape)],
-        out_specs=pl.BlockSpec((rows, 2, 2 * scan_width), lambda j: (j, 0, 0)),
-        out_shape=jax.ShapeDtypeStruct((depth, 2, 2 * scan_width), f32),
+        out_join_kernel,
+        grid_spec=pltpu.PrefetchScalarGridSpec(
+            num_scalar_prefetch=1,
+            grid=(4,),
+            in_specs=[from_four(a) for a in operands],
+            out_specs=pl.BlockSpec((4 * quarter, quarter), lambda j, place: (0, j)),
+        ),
+        out_shape=jax.ShapeDtypeStruct((4 * quarter, 4 * quarter), f32),
         compiler_params=pltpu.CompilerParams(vmem_limit_bytes=vmem_bytes),
-        name="joined",
-    )(first, second, inner)
+        name="joined_out",
+    )(place, *operands)
+
+
+def joined_in(place, first, second, inner):
+    quarter = first[0].shape[1]
+    groups = lax.axis_size("wide") // 4
+    small = inner[0].shape[1] - quarter
+    operands = [*first, *second, *inner]
+    return pl.pallas_call(
+        functools.partial(in_join_kernel, groups=groups),
+        grid_spec=pltpu.PrefetchScalarGridSpec(
+            num_scalar_prefetch=1,
+            grid=(4,),
+            in_specs=[from_four(a) for a in operands],
+            out_specs=[
+                pl.BlockSpec((quarter, 2, 4 * quarter), lambda j, place: (j, 0, 0)),
+                pl.BlockSpec((small, 4 * quarter), lambda j, place: (j, 0)),
+            ],
+        ),
+        out_shape=[
+            jax.ShapeDtypeStruct((4 * quarter, 2, 4 * quarter), f32),
+            jax.ShapeDtypeStruct((4 * small, 4 * quarter), f32),
+        ],
+        compiler_params=pltpu.CompilerParams(vmem_limit_bytes=vmem_bytes),
+        name="joined_in",
+    )(place, *operands)
 
 
 def carried(ends, decay):
@@ -776,10 +917,9 @@
 
     other_tokens = swapped(tokens, "narrow", 1)
     other_cot = swapped(cotangent, "narrow", 1)
-    same_as_last = (segment_ids[rows - halo :] == segment_ids[rows - 1 :])[:, None]
-    edge_rows = jnp.where(same_as_last, tokens[rows - halo :], jnp.zeros((), tokens.dtype))
-    edge, other_edge = to_next_both(edge_rows)
-
+    edge, other_edge = to_next_both(edge_rows_of(segment_ids, tokens))
+
+    same_as_last = (segment_ids[rows - 8 :] == segment_ids[rows - 1 :])[:, None]
     padded_ids = jnp.concatenate([jnp.broadcast_to(segment_ids[:1], (taps - 1,)), segment_ids])
     masks = jnp.stack(
         [
@@ -821,14 +961,14 @@
         )
         here = decay[:, part * scan_width : (part + 1) * scan_width]
         started.append((step_pre, step, carried(ends, here)))
-    normed = normed_ext[:rows]
-    bits = wide_bits()
+    normed_four = quarter_of_four(normed_ext[:rows])
+    cot_four = quarter_of_four(cot_whole)
     select_grad = jnp.zeros(selected.shape, f32)
-    waited = select_grad
+    waits = [[started[-1][2][0]], [normed_four, cot_four]]
     done, sums = [], []
     for part in parts:
         step_pre, step, (entry, tail) = started[part]
-        gated, gate_grad, act_grad, select_grad, small = scan_full(
+        pair, act_grad, select_grad, small = scan_full(
             part,
             selected,
             other_selected,
@@ -844,16 +984,17 @@
             skip_gain[None],
             step_weight,
             select_grad,
-            waited,
+            waits[part],
         )
-        done.append((gated, gate_grad, act_grad, small))
-        waited = first_step([(gated, cot_whole, False), (normed, gate_grad, True)])
-        sums.append(waited)
+        done.append((pair, act_grad, small))
+        sums.append(outer_quarters(*shared_by_four(pair), normed_four, cot_four))
     other_select_grad = swapped(select_grad, "narrow", 1)
-    sums = [gathered(scattered(piece, bits[1:]), bits) for piece in sums]
-    gated, gate_grad, _, scan_small = [
-        jnp.concatenate(pieces, axis=1) for pieces in zip(*done)
-    ]
+    place = (lax.axis_index("wide") & 3).astype(jnp.int32)[None]
+    sums = [shared_by_four(summed_above(piece, 1)) for piece in sums]
+    out_weight_grad = joined_out(place, *sums)
+    scan_small = jnp.concatenate([small for _, _, small in done], axis=1)
+    gated = jnp.concatenate([pair[0] for pair, _, _ in done], axis=1)
+    gate_grad = jnp.concatenate([pair[1] for pair, _, _ in done], axis=1)
 
     def narrow_halves(array):
         low, high = array[:, :features], array[:, features:]
@@ -870,7 +1011,7 @@
             select_grad,
             other_select_grad,
             select_weight,
-            done[part][2],
+            done[part][1],
             convolved,
             act,
             projected,
@@ -881,14 +1022,8 @@
     ]
     inner_main, edges, conv_small = [jnp.concatenate(x, axis=1) for x in zip(*results)]
     from_next = passed_along(edges[:8], "wide", -1)
-    last_rows = edges[8:] + jnp.where(same_as_last[halo - 8 :], from_next, 0.0)
+    last_rows = edges[8:] + jnp.where(same_as_last, from_next, 0.0)
     inner_grad = jnp.concatenate([inner_main[: rows - 8], last_rows.astype(bf16)])
-    inner_piece = first_step(
-        [
-            (normed, inner_grad[:, part * scan_width : (part + 1) * scan_width], True)
-            for part in parts
-        ]
-    )
     normed_part = jnp.einsum(
         "cte,dce->td", jnp.stack([inner_grad, gate_grad]), in_weight, preferred_element_type=f32
     )
@@ -900,10 +1035,18 @@
     small = jnp.concatenate(
         [scan_small, conv_small, gain_part, jnp.zeros((spare, gain_part.shape[1]), f32)]
     )
-    small_mine, small_other = halves_of(small, 0)
-    small_piece = small_mine + swapped(small_other.astype(bf16), "wide", 1).astype(f32)
-    last_piece = scattered(jnp.concatenate([inner_piece, small_piece]), bits[1:])
-    inner_sum = gathered(last_piece, bits)
+    near, far = shared_by_four(inner_grad)
+    inner_four = jnp.concatenate([near, far]).reshape(4 * rows, -1)
+    inner_piece = lax.dot_general(
+        normed_four.reshape(4 * rows, -1), inner_four, contract_first, preferred_element_type=f32
+    )
+    small_piece = scattered(small, (1, 2))
+    groups = lax.axis_size("wide") // 4
+    last_piece = jnp.concatenate(
+        [x.reshape(groups, -1, x.shape[1]) for x in (inner_piece, small_piece)], axis=1
+    ).reshape(-1, inner_piece.shape[1])
+    inner_sum = shared_by_four(summed_above(last_piece, 2))
+    in_weight_grad, small_sum = joined_in(place, *sums, inner_sum)
 
     normed_mine, normed_other = narrow_halves(normed_part)
     row_sum = row_part + swapped(row_part, "narrow", 1)
@@ -914,25 +1057,16 @@
     ) * (row_sum / (2 * features))
     tokens_grad = (whole_grad + cotangent.astype(f32)).astype(bf16)
 
-    core_rows = inner_sum.shape[0] // 2
-    small_at = inner_piece.shape[0]
-    small_sum = jnp.concatenate(
-        [inner_sum[small_at:core_rows], inner_sum[core_rows + small_at :]]
-    ).astype(f32)
     scan_sum = small_sum[: scan_small.shape[0]]
     conv_sum = small_sum[scan_small.shape[0] : scan_small.shape[0] + conv_small.shape[0]]
     gain_row = scan_small.shape[0] + conv_small.shape[0]
     gain_sum = small_sum[gain_row : gain_row + 1]
     norm_gain_grad = (gain_sum + swapped(gain_sum, "narrow", 1))[0]
-    quarter = scan_width // 2
-    out_weight_grad = jnp.concatenate(
-        [x for total in sums for x in (total[:quarter], total[2 * quarter : 3 * quarter])]
-    ).astype(f32)
     return (
         layer_out,
         tokens_grad,
         norm_gain_grad,
-        joined(*sums, inner_sum),
+        in_weight_grad,
         conv_sum[columns : columns + taps],
         conv_sum[columns + taps],
         conv_sum[:columns],

time: 291 us -> 293 us (level)
  waiting for transfers between devices: 105 us -> 78.6 us
  starting transfers between devices: 59.2 us -> 78.4 us
  Pallas kernels: 63.4 us -> 78.9 us
  other arithmetic: 32 us -> 20.6 us
  local copies, waits for them, and re-layouts: 11.1 us -> 21 us
  matrix products: 17.4 us -> 13 us
    ppermute x37 -> x47, waiting for transfers between devices: 104 us -> 76.4 us  [swapped(): return lax.ppermute(array, axis, [(i, i ^ bit) for i in range(peers)])]
    ppermute x37 -> x47, starting transfers between devices: 37.7 us -> 59.5 us  [swapped(): return lax.ppermute(array, axis, [(i, i ^ bit) for i in range(peers)])]
    pallas_call x1 -> x5, Pallas kernels: 6.92 us -> 22.6 us  [the longest x1 8.74 us: joined_in(): pl.pallas_call(functools.partial(in_join_kernel, groups=groups), grid_spe...]
    another operation x0 -> x12, other arithmetic: none -> 5.87 us  [the longest x9 3.87 us: shared_by_four(): near = jnp.stack([array, swapped(array, 'wide', 2)])]
    dot_general x12 -> x1, matrix products: 5.89 us -> 0.7 us  [local(): lax.dot_general(normed_four.reshape(4 * rows, -1), inner_four, contract_f...]
    convert_element_type x14 -> x3, other arithmetic: 4.22 us -> 0.15 us  [summed_above(): held = piece.astype(bf16)]
    add x11 -> x3, other arithmetic: 5.22 us -> 1.28 us  [scattered(): total = total + swapped(block(n).astype(bf16), 'wide', flip).astype(f32)]
    concatenate x15 -> x4, other arithmetic: 5.47 us -> 1.6 us  [the longest x1 1.43 us: local(): inner_four = jnp.concatenate([near, far]).reshape(4 * rows, -1)]
  transfers between devices with their start and end apart: 44 -> 54, of which waited for: 20 -> 17; matrix products, arithmetic and copies ran while one was open for 14% -> 16% of each run, Pallas kernels for 14% -> 22%
where the time goes in v4:
time: 293 us; the launch traced here: 292 us
  Pallas kernels  78.9 us (27%)
  waiting for transfers between devices  78.6 us (27%)
  starting transfers between devices  78.4 us (27%)
  local copies, waits for them, and re-layouts  21 us (7%)
  other arithmetic  20.6 us (7%)
  matrix products  13 us (4%)
    ppermute x47, waiting for transfers between devices, swapped(): return lax.ppermute(array, axis, [(i, i ^ bit) for i in range(peers)])  76.4 us
    ppermute x47, starting transfers between devices, swapped(): return lax.ppermute(array, axis, [(i, i ^ bit) for i in range(peers)])  59.5 us
    pallas_call x7, Pallas kernels, call(): pl.pallas_call(kernel, grid=(width // scan_width,), in_specs=in_specs, ou...  54.1 us
    ppermute x6, starting transfers between devices, passed_along(): return lax.ppermute(array, axis, pairs)  14.8 us
    pallas_call x1, Pallas kernels, joined_in(): pl.pallas_call(functools.partial(in_join_kernel, groups=groups), grid_spe...  8.74 us
    pallas_call x2, Pallas kernels, outer_quarters(): pl.pallas_call(outer_kernel, out_shape=jax.ShapeDtypeStruct((quarter, 4 *...  7.11 us
  transfers between devices with their start and end apart: 54, of which 17 were waited for; matrix products, arithmetic and copies ran while one was open for 16% of the time, Pallas kernels for 22%

profile of v4, /device:TPU:0, one launch (start us, length us, event | category | flops | bytes accessed | tf_op | source)
XLA Modules:
  0.0 292.0 jit_solution(8054629407952000452)
XLA Ops:
  0.7 3.0 %collective-permute-start = (bf16[256,512]{1,0:T(8,128)(2,1)}, bf16[256,512]{1,0:T(8,128)(2,1)S(1)}, u32[]{:S(2)}, u32[]{:S(2)}) collective-permute-start(bf16[256,512]{1,0:T(8,128)(2,1)} %own_ref.1), channel_id=1, source_target_pairs={{0,1},{1,0},{2,3},{3,2},{4,5},{5,4},{6,7},{7,6},{8,9},{9,8},{10,11... | collective-permute-start | bytes 786440 | tf_op jit(solution)/shard_map/ppermute | solution.py:32
  3.7 1.4 edge_rows.1
  5.1 1.4 collective-permute-start.1
  6.5 4.1 %collective-permute-start.2 = (bf16[16,512]{1,0:T(8,128)(2,1)}, bf16[16,512]{1,0:T(8,128)(2,1)S(1)}, u32[]{:S(2)}, u32[]{:S(2)}) collective-permute-start(bf16[16,512]{1,0:T(8,128)(2,1)} %edge_rows.1), channel_id=1, source_target_pairs={{0,3},{1,2},{2,5},{3,4},{4,7},{5,6},{6,9},{7,8},{8,11},{9,10},{10,... | collective-permute-start | bytes 49160 | tf_op jit(solution)/shard_map/ppermute | solution.py:50
  10.7 1.5 collective-permute-start.4
  12.2 1.3 fusion.53
  14.4 1.5 compare_convert_fusion
  15.9 1.4 slice_compare_fusion
  18.9 2.2 normalized.1
  21.1 1.1 slice.183
  22.2 4.9 %fusion.7.inner_ref.gate_ref = bf16[2,272,1024]{2,1,0:T(8,128)(2,1)} fusion(bf16[1024,2,1024]{2,1,0:T(2,128)(2,1)} %param.15, bf16[272,1024]{1,0:T(8,128)(2,1)} %get-tuple-element.40), kind=kOutput, calls=%fused_computation.6 | convolution fusion | flops 1141407744 | bytes 5865472 | tf_op jit(solution)/shard_map/td,dce->cte/dot_general | solution.py:935
  27.1 3.5 %convolve.1 = (f32[256,1024]{1,0:T(8,128)}, bf16[256,1024]{1,0:T(8,128)(2,1)}, f32[96,256]{1,0:T(8,128)}) custom-call(bf16[2,272,1024]{2,1,0:T(8,128)(2,1)} %fusion.7.inner_ref.gate_ref, f32[4,1024]{1,0:T(4,128)} %conv_weight_ref.5, f32[1,1024]{1,0:T(1,128)} %bitcast.144, bf16[96,1024]{1,0:T(8,128)(2,1)} %select_ref.5, f32[256,8]{1,0:T(8,128)} %copy.35.mask_ref), custom_call_target="tpu_custom_call" | custom-call | flops 4000000000 | bytes 1339392 | tf_op jit(solution)/shard_map/convolve/pallas_call | solution.py:143
  31.3 1.7 fusion.25.gated_grad_ref
  33.9 1.2 collective-permute-start.14
  37.2 6.6 %scan_ends.2 = (f32[256,512]{1,0:T(8,128)}, f32[256,512]{1,0:T(8,128)}, f32[40,512]{1,0:T(8,128)}) custom-call(f32[96,256]{1,0:T(8,128)} %get-tuple-element.41.selected_ref, f32[96,256]{1,0:T(8,128)} %copy-done.35, bf16[64,1024]{1,0:T(8,128)(2,1)} %step_weight_ref.7, f32[1,1024]{1,0:T(1,128)} %bitcast.145, bf16[256,1024]{1,0:T(8,128)(2,1)} %get-tuple-element.42.act_ref, ...), custom_call_target="tpu_custom_call" | custom-call | flops 5000000000 | bytes 3092480 | tf_op jit(solution)/shard_map/scan_ends/pallas_call | solution.py:143
  44.7 6.6 %scan_ends.3 = (f32[256,512]{1,0:T(8,128)}, f32[256,512]{1,0:T(8,128)}, f32[40,512]{1,0:T(8,128)}) custom-call(f32[96,256]{1,0:T(8,128)} %get-tuple-element.41.selected_ref, f32[96,256]{1,0:T(8,128)} %copy-done.35, bf16[64,1024]{1,0:T(8,128)(2,1)} %step_weight_ref.7, f32[1,1024]{1,0:T(1,128)} %bitcast.146, bf16[256,1024]{1,0:T(8,128)(2,1)} %get-tuple-element.42.act_ref, ...), custom_call_target="tpu_custom_call" | custom-call | flops 5000000000 | bytes 3092480 | tf_op jit(solution)/shard_map/scan_ends/pallas_call | solution.py:143
  52.2 1.6 collective-permute-start.6
  54.6 4.5 %collective-permute-done.6 = f32[40,512]{1,0:T(8,128)S(1)} collective-permute-done((f32[40,512]{1,0:T(8,128)S(1)}, f32[40,512]{1,0:T(8,128)S(1)}, u32[]{:S(2)}, u32[]{:S(2)}) %collective-permute-start.6) | collective-permute-done | bytes 81952 | tf_op jit(solution)/shard_map/ppermute | solution.py:32
  62.2 1.3 collective-permute-start.8
  63.5 4.5 %collective-permute-start.7 = (f32[16,512]{1,0:T(8,128)S(1)}, f32[16,512]{1,0:T(8,128)S(1)}, u32[]{:S(2)}, u32[]{:S(2)}) collective-permute-start(f32[16,512]{1,0:T(8,128)S(1)} %get-tuple-element.145), channel_id=1, source_target_pairs={{0,8},{2,10},{4,12},{6,14},{8,16},{10,18},{12,20},{14,22},{16,24},... | collective-permute-start | bytes 98312 | tf_op jit(solution)/shard_map/ppermute | solution.py:27
  68.1 1.3 collective-permute-start.12
  69.4 4.7 %collective-permute-start.11 = (f32[16,512]{1,0:T(8,128)S(1)}, f32[16,512]{1,0:T(8,128)S(1)}, u32[]{:S(2)}, u32[]{:S(2)}) collective-permute-start(f32[16,512]{1,0:T(8,128)S(1)} %get-tuple-element.147), channel_id=1, source_target_pairs={{0,8},{2,10},{4,12},{6,14},{8,16},{10,18},{12,20},{14,22},{16,24},... | collective-permute-start | bytes 98312 | tf_op jit(solution)/shard_map/ppermute | solution.py:27
  76.8 15.3 %scan_full.2 = (bf16[2,256,512]{2,1,0:T(8,128)(2,1)}, f32[256,512]{1,0:T(8,128)}, f32[96,256]{1,0:T(8,128)}, f32[96,512]{1,0:T(8,128)}) custom-call(f32[96,256]{1,0:T(8,128)} %get-tuple-element.41.selected_ref, f32[96,256]{1,0:T(8,128)} %copy-done.35, f32[256,512]{1,0:T(8,128)} %get-tuple-element.43.step_pre_ref, f32[256,512]{1,0:T(8,128)} %get-tuple-element.44.step_ref, ...), custom_call_target="tpu_custom_call" | custom-call | flops 12999999488 | bytes 4337664 | tf_op jit(solution)/shard_map/scan_full/pallas_call | solution.py:143
  93.2 1.6 collective-permute-start.24
  94.8 15.4 %scan_full.3 = (bf16[2,256,512]{2,1,0:T(8,128)(2,1)}, f32[256,512]{1,0:T(8,128)}, f32[96,256]{1,0:T(8,128)}, f32[96,512]{1,0:T(8,128)}) custom-call(f32[96,256]{1,0:T(8,128)} %get-tuple-element.41.selected_ref, f32[96,256]{1,0:T(8,128)} %copy-done.35, f32[256,512]{1,0:T(8,128)} %get-tuple-element.48.step_pre_ref, f32[256,512]{1,0:T(8,128)} %get-tuple-element.49.step_ref, ...), custom_call_target="tpu_custom_call" | custom-call | flops 12999999488 | bytes 5353472 | tf_op jit(solution)/shard_map/scan_full/pallas_call | solution.py:143
  110.2 1.5 collective-permute-start.20
  111.6 1.8 slice_bitcast_fusion
  113.9 1.1 collective-permute-done.20.other_ref
  115.7 3.3 %convolve_grad.2 = (bf16[256,512]{1,0:T(8,128)(2,1)}, f32[16,512]{1,0:T(8,128)}, f32[112,512]{1,0:T(8,128)}) custom-call(f32[96,256]{1,0:T(8,128)} %get-tuple-element.53.select_grad_ref, f32[96,256]{1,0:T(8,128)} %copy-done.36, bf16[96,1024]{1,0:T(8,128)(2,1)} %select_ref.5, f32[256,512]{1,0:T(8,128)} %get-tuple-element.54.act_grad_ref, ...), custom_call_target="tpu_custom_call" | custom-call | flops 3000000000 | bytes 3629056 | tf_op jit(solution)/shard_map/convolve_grad/pallas_call | solution.py:143
  119.7 3.3 %convolve_grad.3 = (bf16[256,512]{1,0:T(8,128)(2,1)}, f32[16,512]{1,0:T(8,128)}, f32[112,512]{1,0:T(8,128)}) custom-call(f32[96,256]{1,0:T(8,128)} %get-tuple-element.53.select_grad_ref, f32[96,256]{1,0:T(8,128)} %copy-done.36, bf16[96,1024]{1,0:T(8,128)(2,1)} %select_ref.5, f32[256,512]{1,0:T(8,128)} %get-tuple-element.57.act_grad_ref, ...), custom_call_target="tpu_custom_call" | custom-call | flops 3000000000 | bytes 3629056 | tf_op jit(solution)/shard_map/convolve_grad/pallas_call | solution.py:143
  123.9 1.5 collective-permute-start.21
  125.4 1.5 collective-permute-done.21
  129.0 5.0 %fusion.15 = (f32[1024]{0:T(1024)S(1)}, f32[256]{0:T(256)S(1)}, f32[256,1024]{1,0:T(8,128)}) fusion(f32[256]{0:T(256)S(1)} %get-tuple-element.70, bf16[272,1024]{1,0:T(8,128)(2,1)S(1)} %copy-done.34, f32[1024]{0:T(1024)S(1)} %copy-done.31, bf16[1024,2,1024]{2,1,0:T(2,128)(2,1)} %param.15, bf16[1,256,1024]{2,1,0:T(8,128)(2,1)S(1)} %bitcast.90, ...), kind=kOutput, calls=%fused_computation.16 | convolution fusion | flops 1076099840 | bytes 6825984 | tf_op jit(solution)/shard_map/cte,dce->td/dot_general | solution.py:1027
  135.1 3.1 %collective-permute-start.25 = (bf16[2,2,256,512]{3,2,1,0:T(8,128)(2,1)}, bf16[2,2,256,512]{3,2,1,0:T(8,128)(2,1)}, u32[]{:S(2)}, u32[]{:S(2)}) collective-permute-start(bf16[2,2,256,512]{3,2,1,0:T(8,128)(2,1)} %pad_maximum_fusion.6.near_ref), channel_id=1, source_target_pairs={{0,2},{2,0},{4,6},{6,4},{8,10},{10,8},{12,14},{14,12},{16,18},{18,... | collective-permute-start | bytes 3145736 | tf_op jit(solution)/shard_map/ppermute | solution.py:32
  142.1 1.1 pad_maximum_fusion.3
  143.1 1.5 collective-permute-start.41
  146.9 3.5 %collective-permute-done.43 = bf16[64,1024]{1,0:T(8,128)(2,1)} collective-permute-done((bf16[64,1024]{1,0:T(8,128)(2,1)}, bf16[64,1024]{1,0:T(8,128)(2,1)}, u32[]{:S(2)}, u32[]{:S(2)}) %collective-permute-start.43) | collective-permute-done | bytes 131104 | tf_op jit(solution)/shard_map/ppermute | solution.py:32
  150.3 1.1 convert_add_fusion.3
  151.5 3.6 %outer_quarters.2 = f32[256,1024]{1,0:T(8,128)} custom-call(bf16[2,2,256,512]{3,2,1,0:T(8,128)(2,1)} %pad_maximum_fusion.6.near_ref, bf16[2,2,256,512]{3,2,1,0:T(8,128)(2,1)} %collective-permute-done.25.far_ref, bf16[4,256,256]{2,1,0:T(8,128)(2,1)} %pad_maximum_fusion.13.rest_0_.normed_ref, bf16[4,256,256]{2,1,0:T(8,128)(2,1)} %pad_maximum_fusion.14.rest_1_.cot_ref), custom_call_target="tpu_custom_call" | custom-call | flops 2000000000 | bytes 4000000 | tf_op jit(solution)/shard_map/outer_quarters/pallas_call | solution.py:738
  156.1 3.1 %collective-permute-start.26 = (bf16[128,1024]{1,0:T(8,128)(2,1)S(1)}, bf16[128,1024]{1,0:T(8,128)(2,1)S(1)}, u32[]{:S(2)}, u32[]{:S(2)}) collective-permute-start(bf16[128,1024]{1,0:T(8,128)(2,1)S(1)} %dynamic-slice_convert_fusion.1), channel_id=1, source_target_pairs={{0,8},{2,10},{4,12},{6,14},{8,0},{10,2},{12,4},{14,6},{16,24},{18,... | collective-permute-start | bytes 786440 | tf_op jit(solution)/shard_map/ppermute | solution.py:32
  159.3 3.6 %outer_quarters.3 = f32[256,1024]{1,0:T(8,128)} custom-call(bf16[2,2,256,512]{3,2,1,0:T(8,128)(2,1)} %pad_maximum_fusion.8.near_ref, bf16[2,2,256,512]{3,2,1,0:T(8,128)(2,1)} %collective-permute-done.33.far_ref, bf16[4,256,256]{2,1,0:T(8,128)(2,1)} %pad_maximum_fusion.13.rest_0_.normed_ref, bf16[4,256,256]{2,1,0:T(8,128)(2,1)} %pad_maximum_fusion.14.rest_1_.cot_ref), custom_call_target="tpu_custom_call" | custom-call | flops 2000000000 | bytes 4000000 | tf_op jit(solution)/shard_map/outer_quarters/pallas_call | solution.py:738
  164.0 1.4 pad_maximum_fusion
  166.4 4.3 %collective-permute-start.47 = (bf16[80,1024]{1,0:T(8,128)(2,1)S(1)}, bf16[80,1024]{1,0:T(8,128)(2,1)S(1)}, u32[]{:S(2)}, u32[]{:S(2)}) collective-permute-start(bf16[80,1024]{1,0:T(8,128)(2,1)S(1)} %get-tuple-element.87), channel_id=1, source_target_pairs={{0,24},{2,26},{4,28},{6,30},{8,16},{10,18},{12,20},{14,22},{16,8},... | collective-permute-start | bytes 491528 | tf_op jit(solution)/shard_map/ppermute | solution.py:32
  171.5 2.4 collective-permute-start.27
  174.0 3.1 %collective-permute-start.35 = (bf16[64,1024]{1,0:T(8,128)(2,1)S(1)}, bf16[64,1024]{1,0:T(8,128)(2,1)S(1)}, u32[]{:S(2)}, u32[]{:S(2)}) collective-permute-start(bf16[64,1024]{1,0:T(8,128)(2,1)S(1)} %dynamic-slice_convert_fusion.8), channel_id=1, source_target_pairs={{0,16},{2,18},{4,20},{6,22},{8,24},{10,26},{12,28},{14,30},{16,0},... | collective-permute-start | bytes 393224 | tf_op jit(solution)/shard_map/ppermute | solution.py:32
  177.1 2.0 collective-permute-done.47
  179.1 6.7 %collective-permute-done.46 = bf16[80,1024]{1,0:T(8,128)(2,1)S(1)} collective-permute-done((bf16[80,1024]{1,0:T(8,128)(2,1)S(1)}, bf16[80,1024]{1,0:T(8,128)(2,1)S(1)}, u32[]{:S(2)}, u32[]{:S(2)}) %collective-permute-start.46) | collective-permute-done | bytes 163872 | tf_op jit(solution)/shard_map/ppermute | solution.py:32
  185.9 10.1 %collective-permute-start.50 = (bf16[80,1024]{1,0:T(8,128)(2,1)S(1)}, bf16[80,1024]{1,0:T(8,128)(2,1)S(1)}, u32[]{:S(2)}, u32[]{:S(2)}) collective-permute-start(bf16[80,1024]{1,0:T(8,128)(2,1)S(1)} %add_convert_fusion), channel_id=1, source_target_pairs={{0,8},{2,10},{4,12},{6,14},{8,0},{10,2},{12,4},{14,6},{16,24},{18,... | collective-permute-start | bytes 491528 | tf_op jit(solution)/shard_map/ppermute | solution.py:32
  196.0 2.9 collective-permute-start.48
  199.4 2.5 collective-permute-start.28
  202.5 3.0 %collective-permute-done.48 = bf16[80,1024]{1,0:T(8,128)(2,1)S(1)} collective-permute-done((bf16[80,1024]{1,0:T(8,128)(2,1)S(1)}, bf16[80,1024]{1,0:T(8,128)(2,1)S(1)}, u32[]{:S(2)}, u32[]{:S(2)}) %collective-permute-start.48) | collective-permute-done | bytes 163872 | tf_op jit(solution)/shard_map/ppermute | solution.py:32
  205.6 10.2 %collective-permute-done.49 = bf16[80,1024]{1,0:T(8,128)(2,1)S(1)} collective-permute-done((bf16[80,1024]{1,0:T(8,128)(2,1)S(1)}, bf16[80,1024]{1,0:T(8,128)(2,1)S(1)}, u32[]{:S(2)}, u32[]{:S(2)}) %collective-permute-start.49) | collective-permute-done | bytes 163872 | tf_op jit(solution)/shard_map/ppermute | solution.py:32
  216.6 1.9 collective-permute-done.28
  218.8 1.6 collective-permute-done.36
  220.8 7.1 %collective-permute-done.29 = bf16[128,1024]{1,0:T(8,128)(2,1)S(1)} collective-permute-done((bf16[128,1024]{1,0:T(8,128)(2,1)S(1)}, bf16[128,1024]{1,0:T(8,128)(2,1)S(1)}, u32[]{:S(2)}, u32[]{:S(2)}) %collective-permute-start.29) | collective-permute-done | bytes 262176 | tf_op jit(solution)/shard_map/ppermute | solution.py:32
  228.7 2.8 collective-permute-done.37
  232.5 10.6 %collective-permute-done.30 = bf16[256,1024]{1,0:T(8,128)(2,1)S(1)} collective-permute-done((bf16[256,1024]{1,0:T(8,128)(2,1)S(1)}, bf16[256,1024]{1,0:T(8,128)(2,1)S(1)}, u32[]{:S(2)}, u32[]{:S(2)}) %collective-permute-start.30) | collective-permute-done | bytes 524320 | tf_op jit(solution)/shard_map/ppermute | solution.py:32
  243.3 8.5 %collective-permute-done.38 = bf16[256,1024]{1,0:T(8,128)(2,1)S(1)} collective-permute-done((bf16[256,1024]{1,0:T(8,128)(2,1)S(1)}, bf16[256,1024]{1,0:T(8,128)(2,1)S(1)}, u32[]{:S(2)}, u32[]{:S(2)}) %collective-permute-start.38) | collective-permute-done | bytes 524320 | tf_op jit(solution)/shard_map/ppermute | solution.py:32
  252.9 1.4 collective-permute-start.19
  255.0 12.3 %collective-permute-done.23 = f32[256,1]{0,1:T(1,128)S(1)} collective-permute-done((f32[256,1]{0,1:T(1,128)S(1)}, f32[256,1]{0,1:T(1,128)S(1)}, u32[]{:S(2)}, u32[]{:S(2)}) %collective-permute-start.23) | collective-permute-done | bytes 1056 | tf_op jit(solution)/shard_map/ppermute | solution.py:32
  267.3 1.4 collective-permute-start.22
  270.9 8.7 %joined_in.1 = (f32[1024,2,1024]{2,1,0:T(2,128)}, f32[256,1024]{1,0:T(8,128)}) custom-call(s32[1]{0:T(128)} %bitcast.46.place_ref, bf16[2,256,1024]{2,1,0:T(8,128)(2,1)} %copy-done.1, bf16[2,256,1024]{2,1,0:T(8,128)(2,1)} %copy-done.4, bf16[2,256,1024]{2,1,0:T(8,128)(2,1)} %copy-done.2, bf16[2,256,1024]{2,1,0:T(8,128)(2,1)} %copy-done.5, ...), custom_call_target="tpu_custom_call" | custom-call | tf_op jit(solution)/shard_map/joined_in/pallas_call | solution.py:834
  281.0 2.2 fusion.24
  283.2 5.4 %joined_out.1 = f32[1024,1024]{1,0:T(8,128)} custom-call(s32[1]{0:T(128)} %bitcast.46.place_ref, bf16[2,256,1024]{2,1,0:T(8,128)(2,1)} %copy-done.1, bf16[2,256,1024]{2,1,0:T(8,128)(2,1)} %copy-done.4, bf16[2,256,1024]{2,1,0:T(8,128)(2,1)} %copy-done.2, bf16[2,256,1024]{2,1,0:T(8,128)(2,1)} %copy-done.5), custom_call_target="tpu_custom_call" | custom-call | tf_op jit(solution)/shard_map/joined_out/pallas_call | solution.py:815
  (219 shorter events, 44.6 us)
Async XLA Ops:
  0.6 30.7 %copy-start = (bf16[1024,1024]{1,0:T(8,128)(2,1)S(1)}, bf16[1024,1024]{1,0:T(8,128)(2,1)}, u32[]{:S(2)}) copy-start(bf16[1024,1024]{1,0:T(8,128)(2,1)} %param.23) | copy-start | bytes 6291460
  0.7 17.6 %collective-permute-start = (bf16[256,512]{1,0:T(8,128)(2,1)}, bf16[256,512]{1,0:T(8,128)(2,1)S(1)}, u32[]{:S(2)}, u32[]{:S(2)}) collective-permute-start(bf16[256,512]{1,0:T(8,128)(2,1)} %own_ref.1), channel_id=1, source_target_pairs={{0,1},{1,0},{2,3},{3,2},{4,5},{5,4},{6,7},{7,6},{8,9},{9,8},{10,11... | collective-permute-start | bytes 786440 | tf_op jit(solution)/shard_map/ppermute | solution.py:32
  5.1 13.2 %collective-permute-start.1 = (bf16[16,512]{1,0:T(8,128)(2,1)}, bf16[16,512]{1,0:T(8,128)(2,1)S(1)}, u32[]{:S(2)}, u32[]{:S(2)}) collective-permute-start(bf16[16,512]{1,0:T(8,128)(2,1)} %edge_rows.1), channel_id=1, source_target_pairs={{0,2},{2,4},{4,6},{6,8},{8,10},{10,12},{12,14},{14,16},{16,18},{18... | collective-permute-start | bytes 49160 | tf_op jit(solution)/shard_map/ppermute | solution.py:27
  6.5 11.7 %collective-permute-start.2 = (bf16[16,512]{1,0:T(8,128)(2,1)}, bf16[16,512]{1,0:T(8,128)(2,1)S(1)}, u32[]{:S(2)}, u32[]{:S(2)}) collective-permute-start(bf16[16,512]{1,0:T(8,128)(2,1)} %edge_rows.1), channel_id=1, source_target_pairs={{0,3},{1,2},{2,5},{3,4},{4,7},{5,6},{6,9},{7,8},{8,11},{9,10},{10,... | collective-permute-start | bytes 49160 | tf_op jit(solution)/shard_map/ppermute | solution.py:50
  10.7 20.6 %collective-permute-start.4 = (bf16[256,512]{1,0:T(8,128)(2,1)}, bf16[256,512]{1,0:T(8,128)(2,1)S(1)}, u32[]{:S(2)}, u32[]{:S(2)}) collective-permute-start(bf16[256,512]{1,0:T(8,128)(2,1)} %param.25), channel_id=1, source_target_pairs={{0,1},{1,0},{2,3},{3,2},{4,5},{5,4},{6,7},{7,6},{8,9},{9,8},{10,11... | collective-permute-start | bytes 786440 | tf_op jit(solution)/shard_map/ppermute | solution.py:32
  30.6 6.0 %collective-permute-start.3 = (f32[96,256]{1,0:T(8,128)}, f32[96,256]{1,0:T(8,128)S(1)}, u32[]{:S(2)}, u32[]{:S(2)}) collective-permute-start(f32[96,256]{1,0:T(8,128)} %get-tuple-element.41.selected_ref), channel_id=1, source_target_pairs={{0,1},{1,0},{2,3},{3,2},{4,5},{5,4},{6,7},{7,6},{8,9},{9,8},{10,11... | collective-permute-start | bytes 294920 | tf_op jit(solution)/shard_map/ppermute | solution.py:32
  33.4 18.1 %collective-permute-start.15 = (bf16[256,256]{1,0:T(8,128)(2,1)S(1)}, bf16[256,256]{1,0:T(8,128)(2,1)S(1)}, u32[]{:S(2)}, u32[]{:S(2)}) collective-permute-start(bf16[256,256]{1,0:T(8,128)(2,1)S(1)} %get-tuple-element.117), channel_id=1, source_target_pairs={{0,6},{2,4},{4,2},{6,0},{8,14},{10,12},{12,10},{14,8},{16,22},{18,... | collective-permute-start | bytes 393224 | tf_op jit(solution)/shard_map/ppermute | solution.py:32
  33.9 18.1 %collective-permute-start.14 = (bf16[256,256]{1,0:T(8,128)(2,1)S(1)}, bf16[256,256]{1,0:T(8,128)(2,1)S(1)}, u32[]{:S(2)}, u32[]{:S(2)}) collective-permute-start(bf16[256,256]{1,0:T(8,128)(2,1)S(1)} %get-tuple-element.118), channel_id=1, source_target_pairs={{0,2},{2,0},{4,6},{6,4},{8,10},{10,8},{12,14},{14,12},{16,18},{18,... | collective-permute-start | bytes 393224 | tf_op jit(solution)/shard_map/ppermute | solution.py:32
  35.1 17.1 %collective-permute-start.13 = (bf16[256,256]{1,0:T(8,128)(2,1)S(1)}, bf16[256,256]{1,0:T(8,128)(2,1)S(1)}, u32[]{:S(2)}, u32[]{:S(2)}) collective-permute-start(bf16[256,256]{1,0:T(8,128)(2,1)S(1)} %get-tuple-element.119), channel_id=1, source_target_pairs={{0,4},{2,6},{4,0},{6,2},{8,12},{10,14},{12,8},{14,10},{16,20},{18,... | collective-permute-start | bytes 393224 | tf_op jit(solution)/shard_map/ppermute | solution.py:32
  35.6 25.7 %collective-permute-start.18 = (bf16[256,256]{1,0:T(8,128)(2,1)S(1)}, bf16[256,256]{1,0:T(8,128)(2,1)S(1)}, u32[]{:S(2)}, u32[]{:S(2)}) collective-permute-start(bf16[256,256]{1,0:T(8,128)(2,1)S(1)} %get-tuple-element.115), channel_id=1, source_target_pairs={{0,6},{2,4},{4,2},{6,0},{8,14},{10,12},{12,10},{14,8},{16,22},{18,... | collective-permute-start | bytes 393224 | tf_op jit(solution)/shard_map/ppermute | solution.py:32
  43.9 7.5 %copy-start.30 = (f32[40,512]{1,0:T(8,128)S(1)}, f32[40,512]{1,0:T(8,128)}, u32[]{:S(2)}) copy-start(f32[40,512]{1,0:T(8,128)} %get-tuple-element.45) | copy-start | bytes 245764
  43.9 7.4 %collective-permute-start.5 = (f32[40,512]{1,0:T(8,128)}, f32[40,512]{1,0:T(8,128)S(1)}, u32[]{:S(2)}, u32[]{:S(2)}) collective-permute-start(f32[40,512]{1,0:T(8,128)} %get-tuple-element.45), channel_id=1, source_target_pairs={{0,2},{2,0},{4,6},{6,4},{8,10},{10,8},{12,14},{14,12},{16,18},{18,... | collective-permute-start | bytes 245768 | tf_op jit(solution)/shard_map/ppermute | solution.py:32
  51.3 9.9 %collective-permute-start.17 = (bf16[256,256]{1,0:T(8,128)(2,1)S(1)}, bf16[256,256]{1,0:T(8,128)(2,1)S(1)}, u32[]{:S(2)}, u32[]{:S(2)}) collective-permute-start(bf16[256,256]{1,0:T(8,128)(2,1)S(1)} %get-tuple-element.114), channel_id=1, source_target_pairs={{0,2},{2,0},{4,6},{6,4},{8,10},{10,8},{12,14},{14,12},{16,18},{18,... | collective-permute-start | bytes 393224 | tf_op jit(solution)/shard_map/ppermute | solution.py:32
  51.4 9.8 %collective-permute-start.16 = (bf16[256,256]{1,0:T(8,128)(2,1)S(1)}, bf16[256,256]{1,0:T(8,128)(2,1)S(1)}, u32[]{:S(2)}, u32[]{:S(2)}) collective-permute-start(bf16[256,256]{1,0:T(8,128)(2,1)S(1)} %get-tuple-element.113), channel_id=1, source_target_pairs={{0,4},{2,6},{4,0},{6,2},{8,12},{10,14},{12,8},{14,10},{16,20},{18,... | collective-permute-start | bytes 393224 | tf_op jit(solution)/shard_map/ppermute | solution.py:32
  52.0 2.7 collective-permute-start.9
  52.2 7.0 %collective-permute-start.6 = (f32[40,512]{1,0:T(8,128)S(1)}, f32[40,512]{1,0:T(8,128)S(1)}, u32[]{:S(2)}, u32[]{:S(2)}) collective-permute-start(f32[40,512]{1,0:T(8,128)S(1)} %pad_maximum_fusion.21), channel_id=1, source_target_pairs={{0,4},{2,6},{4,0},{6,2},{8,12},{10,14},{12,8},{14,10},{16,20},{18,... | collective-permute-start | bytes 245768 | tf_op jit(solution)/shard_map/ppermute | solution.py:32
  60.7 7.3 %collective-permute-start.10 = (f32[40,512]{1,0:T(8,128)S(1)}, f32[40,512]{1,0:T(8,128)S(1)}, u32[]{:S(2)}, u32[]{:S(2)}) collective-permute-start(f32[40,512]{1,0:T(8,128)S(1)} %pad_maximum_fusion.22), channel_id=1, source_target_pairs={{0,4},{2,6},{4,0},{6,2},{8,12},{10,14},{12,8},{14,10},{16,20},{18,... | collective-permute-start | bytes 245768 | tf_op jit(solution)/shard_map/ppermute | solution.py:32
  62.2 11.9 %collective-permute-start.8 = (f32[16,512]{1,0:T(8,128)S(1)}, f32[16,512]{1,0:T(8,128)S(1)}, u32[]{:S(2)}, u32[]{:S(2)}) collective-permute-start(f32[16,512]{1,0:T(8,128)S(1)} %get-tuple-element.144), channel_id=1, source_target_pairs={{8,0},{10,2},{12,4},{14,6},{16,8},{18,10},{20,12},{22,14},{24,16},... | collective-permute-start | bytes 98312 | tf_op jit(solution)/shard_map/ppermute | solution.py:27
  63.5 10.7 %collective-permute-start.7 = (f32[16,512]{1,0:T(8,128)S(1)}, f32[16,512]{1,0:T(8,128)S(1)}, u32[]{:S(2)}, u32[]{:S(2)}) collective-permute-start(f32[16,512]{1,0:T(8,128)S(1)} %get-tuple-element.145), channel_id=1, source_target_pairs={{0,8},{2,10},{4,12},{6,14},{8,16},{10,18},{12,20},{14,22},{16,24},... | collective-permute-start | bytes 98312 | tf_op jit(solution)/shard_map/ppermute | solution.py:27
  68.1 6.7 %collective-permute-start.12 = (f32[16,512]{1,0:T(8,128)S(1)}, f32[16,512]{1,0:T(8,128)S(1)}, u32[]{:S(2)}, u32[]{:S(2)}) collective-permute-start(f32[16,512]{1,0:T(8,128)S(1)} %get-tuple-element.146), channel_id=1, source_target_pairs={{8,0},{10,2},{12,4},{14,6},{16,8},{18,10},{20,12},{22,14},{24,16},... | collective-permute-start | bytes 98312 | tf_op jit(solution)/shard_map/ppermute | solution.py:27
  69.4 6.1 %collective-permute-start.11 = (f32[16,512]{1,0:T(8,128)S(1)}, f32[16,512]{1,0:T(8,128)S(1)}, u32[]{:S(2)}, u32[]{:S(2)}) collective-permute-start(f32[16,512]{1,0:T(8,128)S(1)} %get-tuple-element.147), channel_id=1, source_target_pairs={{0,8},{2,10},{4,12},{6,14},{8,16},{10,18},{12,20},{14,22},{16,24},... | collective-permute-start | bytes 98312 | tf_op jit(solution)/shard_map/ppermute | solution.py:27
  93.2 40.8 %collective-permute-start.24 = (bf16[2,256,512]{2,1,0:T(8,128)(2,1)}, bf16[2,256,512]{2,1,0:T(8,128)(2,1)S(1)}, u32[]{:S(2)}, u32[]{:S(2)}) collective-permute-start(bf16[2,256,512]{2,1,0:T(8,128)(2,1)} %get-tuple-element.47), channel_id=1, source_target_pairs={{0,4},{2,6},{4,0},{6,2},{8,12},{10,14},{12,8},{14,10},{16,20},{18,... | collective-permute-start | bytes 1572872 | tf_op jit(solution)/shard_map/ppermute | solution.py:32
  110.2 4.8 %collective-permute-start.20 = (f32[96,256]{1,0:T(8,128)}, f32[96,256]{1,0:T(8,128)S(1)}, u32[]{:S(2)}, u32[]{:S(2)}) collective-permute-start(f32[96,256]{1,0:T(8,128)} %get-tuple-element.53.select_grad_ref), channel_id=1, source_target_pairs={{0,1},{1,0},{2,3},{3,2},{4,5},{5,4},{6,7},{7,6},{8,9},{9,8},{10,11... | collective-permute-start | bytes 294920 | tf_op jit(solution)/shard_map/ppermute | solution.py:32
  113.4 24.8 %collective-permute-start.32 = (bf16[2,256,512]{2,1,0:T(8,128)(2,1)}, bf16[2,256,512]{2,1,0:T(8,128)(2,1)S(1)}, u32[]{:S(2)}, u32[]{:S(2)}) collective-permute-start(bf16[2,256,512]{2,1,0:T(8,128)(2,1)} %get-tuple-element.51), channel_id=1, source_target_pairs={{0,4},{2,6},{4,0},{6,2},{8,12},{10,14},{12,8},{14,10},{16,20},{18,... | collective-permute-start | bytes 1572872 | tf_op jit(solution)/shard_map/ppermute | solution.py:32
  123.9 3.1 %collective-permute-start.21 = (f32[8,1024]{1,0:T(8,128)S(1)}, f32[8,1024]{1,0:T(8,128)S(1)}, u32[]{:S(2)}, u32[]{:S(2)}) collective-permute-start(f32[8,1024]{1,0:T(8,128)S(1)} %slice.224), channel_id=1, source_target_pairs={{2,0},{4,2},{6,4},{8,6},{10,8},{12,10},{14,12},{16,14},{18,16},{20... | collective-permute-start | bytes 98312 | tf_op jit(solution)/shard_map/ppermute | solution.py:27
  128.0 13.2 %collective-permute-start.40 = (bf16[256,1024]{1,0:T(8,128)(2,1)S(1)}, bf16[256,1024]{1,0:T(8,128)(2,1)S(1)}, u32[]{:S(2)}, u32[]{:S(2)}) collective-permute-start(bf16[256,1024]{1,0:T(8,128)(2,1)S(1)} %fusion.27), channel_id=1, source_target_pairs={{0,4},{2,6},{4,0},{6,2},{8,12},{10,14},{12,8},{14,10},{16,20},{18,... | collective-permute-start | bytes 1572872 | tf_op jit(solution)/shard_map/ppermute | solution.py:32
  135.1 16.4 %collective-permute-start.25 = (bf16[2,2,256,512]{3,2,1,0:T(8,128)(2,1)}, bf16[2,2,256,512]{3,2,1,0:T(8,128)(2,1)}, u32[]{:S(2)}, u32[]{:S(2)}) collective-permute-start(bf16[2,2,256,512]{3,2,1,0:T(8,128)(2,1)} %pad_maximum_fusion.6.near_ref), channel_id=1, source_target_pairs={{0,2},{2,0},{4,6},{6,4},{8,10},{10,8},{12,14},{14,12},{16,18},{18,... | collective-permute-start | bytes 3145736 | tf_op jit(solution)/shard_map/ppermute | solution.py:32
  139.3 19.9 %collective-permute-start.33 = (bf16[2,2,256,512]{3,2,1,0:T(8,128)(2,1)}, bf16[2,2,256,512]{3,2,1,0:T(8,128)(2,1)}, u32[]{:S(2)}, u32[]{:S(2)}) collective-permute-start(bf16[2,2,256,512]{3,2,1,0:T(8,128)(2,1)} %pad_maximum_fusion.8.near_ref), channel_id=1, source_target_pairs={{0,2},{2,0},{4,6},{6,4},{8,10},{10,8},{12,14},{14,12},{16,18},{18,... | collective-permute-start | bytes 3145736 | tf_op jit(solution)/shard_map/ppermute | solution.py:32
  140.3 5.2 %collective-permute-start.44 = (bf16[64,1024]{1,0:T(8,128)(2,1)S(1)}, bf16[64,1024]{1,0:T(8,128)(2,1)S(1)}, u32[]{:S(2)}, u32[]{:S(2)}) collective-permute-start(bf16[64,1024]{1,0:T(8,128)(2,1)S(1)} %get-tuple-element.94), channel_id=1, source_target_pairs={{0,6},{2,4},{4,2},{6,0},{8,14},{10,12},{12,10},{14,8},{16,22},{18,... | collective-permute-start | bytes 393224 | tf_op jit(solution)/shard_map/ppermute | solution.py:32
  143.1 20.9 %collective-permute-start.41 = (bf16[2,256,1024]{2,1,0:T(8,128)(2,1)}, bf16[2,256,1024]{2,1,0:T(8,128)(2,1)}, u32[]{:S(2)}, u32[]{:S(2)}) collective-permute-start(bf16[2,256,1024]{2,1,0:T(8,128)(2,1)} %pad_maximum_fusion.3), channel_id=1, source_target_pairs={{0,2},{2,0},{4,6},{6,4},{8,10},{10,8},{12,14},{14,12},{16,18},{18,... | collective-permute-start | bytes 3145736 | tf_op jit(solution)/shard_map/ppermute | solution.py:32
  144.6 5.7 %collective-permute-start.43 = (bf16[64,1024]{1,0:T(8,128)(2,1)}, bf16[64,1024]{1,0:T(8,128)(2,1)}, u32[]{:S(2)}, u32[]{:S(2)}) collective-permute-start(bf16[64,1024]{1,0:T(8,128)(2,1)} %get-tuple-element.95), channel_id=1, source_target_pairs={{0,4},{2,6},{4,0},{6,2},{8,12},{10,14},{12,8},{14,10},{16,20},{18,... | collective-permute-start | bytes 393224 | tf_op jit(solution)/shard_map/ppermute | solution.py:32
  145.5 4.8 %collective-permute-start.42 = (bf16[64,1024]{1,0:T(8,128)(2,1)}, bf16[64,1024]{1,0:T(8,128)(2,1)}, u32[]{:S(2)}, u32[]{:S(2)}) collective-permute-start(bf16[64,1024]{1,0:T(8,128)(2,1)} %get-tuple-element.93), channel_id=1, source_target_pairs={{0,2},{2,0},{4,6},{6,4},{8,10},{10,8},{12,14},{14,12},{16,18},{18,... | collective-permute-start | bytes 393224 | tf_op jit(solution)/shard_map/ppermute | solution.py:32
  156.1 7.9 %copy-start.14 = (bf16[256,1024]{1,0:T(8,128)(2,1)S(1)}, bf16[256,1024]{1,0:T(8,128)(2,1)}, u32[]{:S(2)}) copy-start(bf16[256,1024]{1,0:T(8,128)(2,1)} %copy-done.13) | copy-start | bytes 1572868
  156.1 15.3 %collective-permute-start.26 = (bf16[128,1024]{1,0:T(8,128)(2,1)S(1)}, bf16[128,1024]{1,0:T(8,128)(2,1)S(1)}, u32[]{:S(2)}, u32[]{:S(2)}) collective-permute-start(bf16[128,1024]{1,0:T(8,128)(2,1)S(1)} %dynamic-slice_convert_fusion.1), channel_id=1, source_target_pairs={{0,8},{2,10},{4,12},{6,14},{8,0},{10,2},{12,4},{14,6},{16,24},{18,... | collective-permute-start | bytes 786440 | tf_op jit(solution)/shard_map/ppermute | solution.py:32
  163.9 10.0 %collective-permute-start.34 = (bf16[128,1024]{1,0:T(8,128)(2,1)S(1)}, bf16[128,1024]{1,0:T(8,128)(2,1)S(1)}, u32[]{:S(2)}, u32[]{:S(2)}) collective-permute-start(bf16[128,1024]{1,0:T(8,128)(2,1)S(1)} %dynamic-slice_convert_fusion), channel_id=1, source_target_pairs={{0,8},{2,10},{4,12},{6,14},{8,0},{10,2},{12,4},{14,6},{16,24},{18,... | collective-permute-start | bytes 786440 | tf_op jit(solution)/shard_map/ppermute | solution.py:32
  166.2 7.7 %copy-start.19 = (f32[256,1024]{1,0:T(8,128)S(1)}, f32[256,1024]{1,0:T(8,128)}, u32[]{:S(2)}) copy-start(f32[256,1024]{1,0:T(8,128)} %outer_quarters.3) | copy-start | bytes 3145732
  166.4 12.7 %collective-permute-start.47 = (bf16[80,1024]{1,0:T(8,128)(2,1)S(1)}, bf16[80,1024]{1,0:T(8,128)(2,1)S(1)}, u32[]{:S(2)}, u32[]{:S(2)}) collective-permute-start(bf16[80,1024]{1,0:T(8,128)(2,1)S(1)} %get-tuple-element.87), channel_id=1, source_target_pairs={{0,24},{2,26},{4,28},{6,30},{8,16},{10,18},{12,20},{14,22},{16,8},... | collective-permute-start | bytes 491528 | tf_op jit(solution)/shard_map/ppermute | solution.py:32
  170.8 15.1 %collective-permute-start.46 = (bf16[80,1024]{1,0:T(8,128)(2,1)S(1)}, bf16[80,1024]{1,0:T(8,128)(2,1)S(1)}, u32[]{:S(2)}, u32[]{:S(2)}) collective-permute-start(bf16[80,1024]{1,0:T(8,128)(2,1)S(1)} %get-tuple-element.88), channel_id=1, source_target_pairs={{0,16},{2,18},{4,20},{6,22},{8,24},{10,26},{12,28},{14,30},{16,0},... | collective-permute-start | bytes 491528 | tf_op jit(solution)/shard_map/ppermute | solution.py:32
  170.8 15.1 %collective-permute-start.45 = (bf16[80,1024]{1,0:T(8,128)(2,1)S(1)}, bf16[80,1024]{1,0:T(8,128)(2,1)S(1)}, u32[]{:S(2)}, u32[]{:S(2)}) collective-permute-start(bf16[80,1024]{1,0:T(8,128)(2,1)S(1)} %get-tuple-element.86), channel_id=1, source_target_pairs={{0,8},{2,10},{4,12},{6,14},{8,0},{10,2},{12,4},{14,6},{16,24},{18,... | collective-permute-start | bytes 491528 | tf_op jit(solution)/shard_map/ppermute | solution.py:32
  171.5 27.9 %collective-permute-start.27 = (bf16[64,1024]{1,0:T(8,128)(2,1)S(1)}, bf16[64,1024]{1,0:T(8,128)(2,1)S(1)}, u32[]{:S(2)}, u32[]{:S(2)}) collective-permute-start(bf16[64,1024]{1,0:T(8,128)(2,1)S(1)} %dynamic-slice_convert_fusion.9), channel_id=1, source_target_pairs={{0,16},{2,18},{4,20},{6,22},{8,24},{10,26},{12,28},{14,30},{16,0},... | collective-permute-start | bytes 393224 | tf_op jit(solution)/shard_map/ppermute | solution.py:32
  174.0 27.9 %collective-permute-start.35 = (bf16[64,1024]{1,0:T(8,128)(2,1)S(1)}, bf16[64,1024]{1,0:T(8,128)(2,1)S(1)}, u32[]{:S(2)}, u32[]{:S(2)}) collective-permute-start(bf16[64,1024]{1,0:T(8,128)(2,1)S(1)} %dynamic-slice_convert_fusion.8), channel_id=1, source_target_pairs={{0,16},{2,18},{4,20},{6,22},{8,24},{10,26},{12,28},{14,30},{16,0},... | collective-permute-start | bytes 393224 | tf_op jit(solution)/shard_map/ppermute | solution.py:32
  185.9 16.6 %collective-permute-start.50 = (bf16[80,1024]{1,0:T(8,128)(2,1)S(1)}, bf16[80,1024]{1,0:T(8,128)(2,1)S(1)}, u32[]{:S(2)}, u32[]{:S(2)}) collective-permute-start(bf16[80,1024]{1,0:T(8,128)(2,1)S(1)} %add_convert_fusion), channel_id=1, source_target_pairs={{0,8},{2,10},{4,12},{6,14},{8,0},{10,2},{12,4},{14,6},{16,24},{18,... | collective-permute-start | bytes 491528 | tf_op jit(solution)/shard_map/ppermute | solution.py:32
  196.0 9.6 %collective-permute-start.48 = (bf16[80,1024]{1,0:T(8,128)(2,1)S(1)}, bf16[80,1024]{1,0:T(8,128)(2,1)S(1)}, u32[]{:S(2)}, u32[]{:S(2)}) collective-permute-start(bf16[80,1024]{1,0:T(8,128)(2,1)S(1)} %add_convert_fusion), channel_id=1, source_target_pairs={{0,24},{2,26},{4,28},{6,30},{8,16},{10,18},{12,20},{14,22},{16,8},... | collective-permute-start | bytes 491528 | tf_op jit(solution)/shard_map/ppermute | solution.py:32
  198.9 16.8 %collective-permute-start.49 = (bf16[80,1024]{1,0:T(8,128)(2,1)S(1)}, bf16[80,1024]{1,0:T(8,128)(2,1)S(1)}, u32[]{:S(2)}, u32[]{:S(2)}) collective-permute-start(bf16[80,1024]{1,0:T(8,128)(2,1)S(1)} %add_convert_fusion), channel_id=1, source_target_pairs={{0,16},{2,18},{4,20},{6,22},{8,24},{10,26},{12,28},{14,30},{16,0},... | collective-permute-start | bytes 491528 | tf_op jit(solution)/shard_map/ppermute | solution.py:32
  199.4 19.1 %collective-permute-start.28 = (bf16[64,1024]{1,0:T(8,128)(2,1)S(1)}, bf16[64,1024]{1,0:T(8,128)(2,1)S(1)}, u32[]{:S(2)}, u32[]{:S(2)}) collective-permute-start(bf16[64,1024]{1,0:T(8,128)(2,1)S(1)} %add_convert_fusion.2), channel_id=1, source_target_pairs={{0,16},{2,18},{4,20},{6,22},{8,24},{10,26},{12,28},{14,30},{16,0},... | collective-permute-start | bytes 393224 | tf_op jit(solution)/shard_map/ppermute | solution.py:32
  201.9 18.4 %collective-permute-start.36 = (bf16[64,1024]{1,0:T(8,128)(2,1)S(1)}, bf16[64,1024]{1,0:T(8,128)(2,1)S(1)}, u32[]{:S(2)}, u32[]{:S(2)}) collective-permute-start(bf16[64,1024]{1,0:T(8,128)(2,1)S(1)} %add_convert_fusion.1), channel_id=1, source_target_pairs={{0,16},{2,18},{4,20},{6,22},{8,24},{10,26},{12,28},{14,30},{16,0},... | collective-permute-start | bytes 393224 | tf_op jit(solution)/shard_map/ppermute | solution.py:32
  216.0 16.3 %collective-permute-start.51 = (bf16[320,1024]{1,0:T(8,128)(2,1)S(1)}, bf16[320,1024]{1,0:T(8,128)(2,1)S(1)}, u32[]{:S(2)}, u32[]{:S(2)}) collective-permute-start(bf16[320,1024]{1,0:T(8,128)(2,1)S(1)} %get-tuple-element.97), channel_id=1, source_target_pairs={{0,4},{2,6},{4,0},{6,2},{8,12},{10,14},{12,8},{14,10},{16,20},{18,... | collective-permute-start | bytes 1966088 | tf_op jit(solution)/shard_map/ppermute | solution.py:32
  218.6 9.3 %collective-permute-start.29 = (bf16[128,1024]{1,0:T(8,128)(2,1)S(1)}, bf16[128,1024]{1,0:T(8,128)(2,1)S(1)}, u32[]{:S(2)}, u32[]{:S(2)}) collective-permute-start(bf16[128,1024]{1,0:T(8,128)(2,1)S(1)} %pad_maximum_fusion.19), channel_id=1, source_target_pairs={{0,8},{2,10},{4,12},{6,14},{8,0},{10,2},{12,4},{14,6},{16,24},{18,... | collective-permute-start | bytes 786440 | tf_op jit(solution)/shard_map/ppermute | solution.py:32
  220.4 11.1 %collective-permute-start.37 = (bf16[128,1024]{1,0:T(8,128)(2,1)S(1)}, bf16[128,1024]{1,0:T(8,128)(2,1)S(1)}, u32[]{:S(2)}, u32[]{:S(2)}) collective-permute-start(bf16[128,1024]{1,0:T(8,128)(2,1)S(1)} %pad_maximum_fusion.20), channel_id=1, source_target_pairs={{0,8},{2,10},{4,12},{6,14},{8,0},{10,2},{12,4},{14,6},{16,24},{18,... | collective-permute-start | bytes 786440 | tf_op jit(solution)/shard_map/ppermute | solution.py:32
  228.1 14.9 %collective-permute-start.30 = (bf16[256,1024]{1,0:T(8,128)(2,1)S(1)}, bf16[256,1024]{1,0:T(8,128)(2,1)S(1)}, u32[]{:S(2)}, u32[]{:S(2)}) collective-permute-start(bf16[256,1024]{1,0:T(8,128)(2,1)S(1)} %get-tuple-element.105), channel_id=1, source_target_pairs={{0,4},{2,6},{4,0},{6,2},{8,12},{10,14},{12,8},{14,10},{16,20},{18,... | collective-permute-start | bytes 1572872 | tf_op jit(solution)/shard_map/ppermute | solution.py:32
  231.8 20.0 %collective-permute-start.38 = (bf16[256,1024]{1,0:T(8,128)(2,1)S(1)}, bf16[256,1024]{1,0:T(8,128)(2,1)S(1)}, u32[]{:S(2)}, u32[]{:S(2)}) collective-permute-start(bf16[256,1024]{1,0:T(8,128)(2,1)S(1)} %get-tuple-element.101), channel_id=1, source_target_pairs={{0,4},{2,6},{4,0},{6,2},{8,12},{10,14},{12,8},{14,10},{16,20},{18,... | collective-permute-start | bytes 1572872 | tf_op jit(solution)/shard_map/ppermute | solution.py:32
  232.4 19.4 %copy-start.3 = (bf16[2,320,1024]{2,1,0:T(8,128)(2,1)}, bf16[2,320,1024]{2,1,0:T(8,128)(2,1)S(1)}, u32[]{:S(2)}) copy-start(bf16[2,320,1024]{2,1,0:T(8,128)(2,1)S(1)} %pad_maximum_fusion.2.inner_near) | copy-start | bytes 3932164
  232.4 36.3 %collective-permute-start.52 = (bf16[2,320,1024]{2,1,0:T(8,128)(2,1)S(1)}, bf16[2,320,1024]{2,1,0:T(8,128)(2,1)S(1)}, u32[]{:S(2)}, u32[]{:S(2)}) collective-permute-start(bf16[2,320,1024]{2,1,0:T(8,128)(2,1)S(1)} %pad_maximum_fusion.2.inner_near), channel_id=1, source_target_pairs={{0,2},{2,0},{4,6},{6,4},{8,10},{10,8},{12,14},{14,12},{16,18},{18,... | collective-permute-start | bytes 3932168 | tf_op jit(solution)/shard_map/ppermute | solution.py:32
  243.1 8.9 %copy-start.16 = (bf16[256,512]{1,0:T(8,128)(2,1)S(1)}, bf16[256,512]{1,0:T(8,128)(2,1)}, u32[]{:S(2)}) copy-start(bf16[256,512]{1,0:T(8,128)(2,1)} %get-tuple-element.111) | copy-start | bytes 786436
  243.2 9.5 %copy-start.1 = (bf16[2,256,1024]{2,1,0:T(8,128)(2,1)}, bf16[2,256,1024]{2,1,0:T(8,128)(2,1)S(1)}, u32[]{:S(2)}) copy-start(bf16[2,256,1024]{2,1,0:T(8,128)(2,1)S(1)} %pad_maximum_fusion.7.first_near) | copy-start | bytes 3145732
  243.2 25.6 %collective-permute-start.31 = (bf16[2,256,1024]{2,1,0:T(8,128)(2,1)S(1)}, bf16[2,256,1024]{2,1,0:T(8,128)(2,1)S(1)}, u32[]{:S(2)}, u32[]{:S(2)}) collective-permute-start(bf16[2,256,1024]{2,1,0:T(8,128)(2,1)S(1)} %pad_maximum_fusion.7.first_near), channel_id=1, source_target_pairs={{0,2},{2,0},{4,6},{6,4},{8,10},{10,8},{12,14},{14,12},{16,18},{18,... | collective-permute-start | bytes 3145736 | tf_op jit(solution)/shard_map/ppermute | solution.py:32
  251.9 16.9 %collective-permute-start.39 = (bf16[2,256,1024]{2,1,0:T(8,128)(2,1)S(1)}, bf16[2,256,1024]{2,1,0:T(8,128)(2,1)S(1)}, u32[]{:S(2)}, u32[]{:S(2)}) collective-permute-start(bf16[2,256,1024]{2,1,0:T(8,128)(2,1)S(1)} %pad_maximum_fusion.9.second_near), channel_id=1, source_target_pairs={{0,2},{2,0},{4,6},{6,4},{8,10},{10,8},{12,14},{14,12},{16,18},{18,... | collective-permute-start | bytes 3145736 | tf_op jit(solution)/shard_map/ppermute | solution.py:32
  252.9 28.1 %collective-permute-start.19 = (f32[256,512]{1,0:T(8,128)S(1)}, f32[256,512]{1,0:T(8,128)}, u32[]{:S(2)}, u32[]{:S(2)}) collective-permute-start(f32[256,512]{1,0:T(8,128)S(1)} %slice_select_fusion.1), channel_id=1, source_target_pairs={{0,1},{1,0},{2,3},{3,2},{4,5},{5,4},{6,7},{7,6},{8,9},{9,8},{10,11... | collective-permute-start | bytes 1572872 | tf_op jit(solution)/shard_map/ppermute | solution.py:32
  254.3 13.0 %collective-permute-start.23 = (f32[256,1]{0,1:T(1,128)S(1)}, f32[256,1]{0,1:T(1,128)S(1)}, u32[]{:S(2)}, u32[]{:S(2)}) collective-permute-start(f32[256,1]{0,1:T(1,128)S(1)} %bitcast.142), channel_id=1, source_target_pairs={{0,1},{1,0},{2,3},{3,2},{4,5},{5,4},{6,7},{7,6},{8,9},{9,8},{10,11... | collective-permute-start | bytes 3080 | tf_op jit(solution)/shard_map/ppermute | solution.py:32
  267.3 13.7 %collective-permute-start.22 = (f32[256,512]{1,0:T(8,128)S(1)}, f32[256,512]{1,0:T(8,128)}, u32[]{:S(2)}, u32[]{:S(2)}) collective-permute-start(f32[256,512]{1,0:T(8,128)S(1)} %slice_select_fusion), channel_id=1, source_target_pairs={{0,1},{1,0},{2,3},{3,2},{4,5},{5,4},{6,7},{7,6},{8,9},{9,8},{10,11... | collective-permute-start | bytes 1572872 | tf_op jit(solution)/shard_map/ppermute | solution.py:32
  270.9 10.1 %copy-start.7 = (f32[256,1024]{1,0:T(8,128)S(1)}, f32[256,1024]{1,0:T(8,128)}, u32[]{:S(2)}) copy-start(f32[256,1024]{1,0:T(8,128)} %get-tuple-element.163) | copy-start | bytes 3145732
  270.9 10.1 %copy-start.9 = (bf16[256,512]{1,0:T(8,128)(2,1)S(1)}, bf16[256,512]{1,0:T(8,128)(2,1)}, u32[]{:S(2)}) copy-start(bf16[256,512]{1,0:T(8,128)(2,1)} %own_ref.1) | copy-start | bytes 786436
  270.9 10.1 %copy-start.18 = (bf16[256,512]{1,0:T(8,128)(2,1)S(1)}, bf16[256,512]{1,0:T(8,128)(2,1)}, u32[]{:S(2)}) copy-start(bf16[256,512]{1,0:T(8,128)(2,1)} %param.25) | copy-start | bytes 786436
  280.4 11.0 %collective-permute-start.53 = (f32[1,1024]{1,0:T(1,128)S(1)}, f32[1,1024]{1,0:T(1,128)S(1)}, u32[]{:S(2)}, u32[]{:S(2)}) collective-permute-start(f32[1,1024]{1,0:T(1,128)S(1)} %slice.199), channel_id=1, source_target_pairs={{0,1},{1,0},{2,3},{3,2},{4,5},{5,4},{6,7},{7,6},{8,9},{9,8},{10,11... | collective-permute-start | bytes 12296 | tf_op jit(solution)/shard_map/ppermute | solution.py:32
  (27 other events, 90.9 us)

commit v5 on v4

--- a/solution.py
+++ b/solution.py
@@ -89,20 +89,6 @@
             for a, b in zip(blocks[0::2], blocks[1::2])
         ]
     return blocks[0]
-
-
-def summed_above(piece, size):
-    for bits in group_bits(size):
-        piece = scattered(piece, bits)
-    held = piece.astype(bf16)
-    for bits in reversed(group_bits(size)):
-        held = gathered(held, bits)
-    return held
-
-
-def shared_by_four(array):
-    near = jnp.stack([array, swapped(array, "wide", 2)])
-    return near, swapped(near, "wide", 1)
 
 
 def quarter_of_four(array):
@@ -720,135 +706,97 @@
     )(ids, tokens)
 
 
-def outer_kernel(near_ref, far_ref, normed_ref, cot_ref, out_ref):
-    quarter = cot_ref.shape[2]
-    out_sum, gate_sum = None, None
-    for n, pair in enumerate((near_ref[0], near_ref[1], far_ref[0], far_ref[1])):
-        first = lax.dot_general(pair[0], cot_ref[n], contract_first, preferred_element_type=f32)
-        second = lax.dot_general(normed_ref[n], pair[1], contract_first, preferred_element_type=f32)
-        out_sum = first if out_sum is None else out_sum + first
-        gate_sum = second if gate_sum is None else gate_sum + second
-    out_ref[:, :quarter] = out_sum[:quarter]
-    out_ref[:, quarter : 2 * quarter] = out_sum[quarter:]
-    out_ref[:, 2 * quarter :] = gate_sum
-
-
-def outer_quarters(near, far, normed, cot):
-    quarter = cot.shape[2]
+def quarter_kernel(
+    place_ref, own_ref, near_ref, far_ref, last_ref, normed_ref, small_ref, keep_ref, send_refs, piece
+):
+    total = None
+    for n, grads in enumerate((own_ref, near_ref, far_ref, last_ref)):
+        part = lax.dot_general(normed_ref[n], grads[...], contract_first, preferred_element_type=f32)
+        total = part if total is None else total + part
+    piece[...] = total
+    for n in range(4):
+        block = place_ref[0] ^ n
+        rows, spare = piece.shape[0] // 4, small_ref.shape[0] // 4
+        inner = piece[pl.ds(pl.multiple_of(block * rows, rows), rows), :]
+        small = small_ref[pl.ds(pl.multiple_of(block * spare, spare), spare), :]
+        if n == 0:
+            keep_ref[:rows, :] = inner
+            keep_ref[rows:, :] = small
+        else:
+            send_refs[n - 1, :rows, :] = inner.astype(bf16)
+            send_refs[n - 1, rows:, :] = small.astype(bf16)
+
+
+def inner_quarter(place, own, near, far, last, normed, small):
+    width = own.shape[1]
+    quarter = normed.shape[2]
+    rows = (quarter + small.shape[0]) // 4
     return pl.pallas_call(
-        outer_kernel,
-        out_shape=jax.ShapeDtypeStruct((quarter, 4 * quarter), f32),
+        quarter_kernel,
+        in_specs=[pl.BlockSpec(memory_space=pltpu.SMEM)]
+        + [pl.BlockSpec(memory_space=pltpu.VMEM)] * 6,
+        out_shape=[
+            jax.ShapeDtypeStruct((rows, width), f32),
+            jax.ShapeDtypeStruct((3, rows, width), bf16),
+        ],
+        scratch_shapes=[pltpu.VMEM((quarter, width), f32)],
         compiler_params=pltpu.CompilerParams(vmem_limit_bytes=vmem_bytes),
         cost_estimate=pl.CostEstimate(
             flops=2_000_000_000, bytes_accessed=4_000_000, transcendentals=0
         ),
-        name="outer_quarters",
-    )(near, far, normed, cot)
-
-
-def select_block(step, place, refs, use):
-    flip = place ^ step
-    for core in range(2):
-
-        @pl.when((flip & 1) == core)
-        def _():
-            use([ref[core] for ref in refs])
-
-
-def out_join_kernel(place_ref, first_near, first_far, second_near, second_far, out_ref):
-    quarter = out_ref.shape[1]
-
-    def use(blocks):
-        for part, block in enumerate(blocks):
-            for lane in range(2):
-                at = (2 * part + lane) * quarter
-                out_ref[at : at + quarter, :] = block[0, :, lane * quarter : (lane + 1) * quarter].astype(f32)
-
-    select_block(
-        pl.program_id(0), place_ref[0], [(first_near, first_far), (second_near, second_far)], use
-    )
-
-
-def in_join_kernel(
-    place_ref,
-    first_near,
-    first_far,
-    second_near,
-    second_far,
-    inner_near,
-    inner_far,
-    out_ref,
-    small_ref,
-    *,
-    groups,
-):
-    rows, half = out_ref.shape[0], out_ref.shape[2] // 2
-    piece = inner_near.shape[1] // groups
-    inner_rows = rows // groups
-    spare = piece - inner_rows
-
-    def use(blocks):
-        first, second, inner = blocks
-        out_ref[:, 1, :half] = first[0, :, half:].astype(f32)
-        out_ref[:, 1, half:] = second[0, :, half:].astype(f32)
-        for n in range(groups):
-            at = n * piece
-            block = inner[0, at : at + piece, :].astype(f32)
-            out_ref[n * inner_rows : (n + 1) * inner_rows, 0, :] = block[:inner_rows]
-            small_ref[n * spare : (n + 1) * spare, :] = block[inner_rows:]
-
-    select_block(
-        pl.program_id(0),
-        place_ref[0],
-        [(first_near, first_far), (second_near, second_far), (inner_near, inner_far)],
-        use,
-    )
-
-
-def from_four(array):
-    return pl.BlockSpec((1,) + array.shape[1:], lambda j, place: ((place[0] ^ j) // 2, 0, 0))
-
-
-def joined_out(place, first, second):
-    quarter = first[0].shape[1]
-    operands = [*first, *second]
+        name="inner_quarter",
+    )(place, own, near, far, last, normed, small)
+
+
+def join_kernel(place_ref, first_ref, second_ref, inner_ref, *rest):
+    out_ref, small_ref = rest[-2:]
+    half = out_ref.shape[2] // 2
+    rows, spare = out_ref.shape[0] // 2, small_ref.shape[0] // 2
+    out_ref[:, 1, :half] = first_ref[...].astype(f32)
+    out_ref[:, 1, half:] = second_ref[...].astype(f32)
+    for n in range(2):
+        at = n * (rows + spare)
+        block = inner_ref[at : at + rows + spare, :].astype(f32)
+        out_ref[n * rows : (n + 1) * rows, 0, :] = block[:rows]
+        small_ref[n * spare : (n + 1) * spare, :] = block[rows:]
+
+
+def joined(place, flip, first, second, inner, before, waits):
+    depth = first.shape[0]
+    quarter, width = depth // 4, 2 * scan_width
+    small = inner.shape[0] - quarter
+
+    def source(j, place):
+        number = place[0] ^ flip
+        return 4 + 2 * lax.rem(number, 2) + j, number // 2
+
+    untouched = [*before, *waits]
     return pl.pallas_call(
-        out_join_kernel,
+        join_kernel,
         grid_spec=pltpu.PrefetchScalarGridSpec(
             num_scalar_prefetch=1,
-            grid=(4,),
-            in_specs=[from_four(a) for a in operands],
-            out_specs=pl.BlockSpec((4 * quarter, quarter), lambda j, place: (0, j)),
-        ),
-        out_shape=jax.ShapeDtypeStruct((4 * quarter, 4 * quarter), f32),
-        compiler_params=pltpu.CompilerParams(vmem_limit_bytes=vmem_bytes),
-        name="joined_out",
-    )(place, *operands)
-
-
-def joined_in(place, first, second, inner):
-    quarter = first[0].shape[1]
-    groups = lax.axis_size("wide") // 4
-    small = inner[0].shape[1] - quarter
-    operands = [*first, *second, *inner]
-    return pl.pallas_call(
-        functools.partial(in_join_kernel, groups=groups),
-        grid_spec=pltpu.PrefetchScalarGridSpec(
-            num_scalar_prefetch=1,
-            grid=(4,),
-            in_specs=[from_four(a) for a in operands],
+            grid=(2,),
+            in_specs=[
+                pl.BlockSpec((quarter // 2, scan_width), source),
+                pl.BlockSpec((quarter // 2, scan_width), source),
+                pl.BlockSpec((inner.shape[0] // 2, width), lambda j, place: (j, 0)),
+            ]
+            + [pl.BlockSpec(memory_space=pl.ANY)] * len(untouched),
             out_specs=[
-                pl.BlockSpec((quarter, 2, 4 * quarter), lambda j, place: (j, 0, 0)),
-                pl.BlockSpec((small, 4 * quarter), lambda j, place: (j, 0)),
+                pl.BlockSpec(
+                    (quarter // 2, 2, width), lambda j, place: (2 * (place[0] ^ flip) + j, 0, 0)
+                ),
+                pl.BlockSpec((small // 2, width), lambda j, place: (2 * (place[0] ^ flip) + j, 0)),
             ],
         ),
         out_shape=[
-            jax.ShapeDtypeStruct((4 * quarter, 2, 4 * quarter), f32),
-            jax.ShapeDtypeStruct((4 * small, 4 * quarter), f32),
-        ],
+            jax.ShapeDtypeStruct((depth, 2, width), f32),
+            jax.ShapeDtypeStruct((4 * small, width), f32),
+        ],
+        input_output_aliases={4 + k: k for k in range(len(before))},
         compiler_params=pltpu.CompilerParams(vmem_limit_bytes=vmem_bytes),
-        name="joined_in",
-    )(place, *operands)
+        name="joined",
+    )(place, first, second, inner, *untouched)
 
 
 def carried(ends, decay):
@@ -961,10 +909,10 @@
         )
         here = decay[:, part * scan_width : (part + 1) * scan_width]
         started.append((step_pre, step, carried(ends, here)))
-    normed_four = quarter_of_four(normed_ext[:rows])
-    cot_four = quarter_of_four(cot_whole)
+    normed = normed_ext[:rows]
+    normed_four = quarter_of_four(normed)
     select_grad = jnp.zeros(selected.shape, f32)
-    waits = [[started[-1][2][0]], [normed_four, cot_four]]
+    waits = [[started[-1][2][0]], [normed_four]]
     done, sums = [], []
     for part in parts:
         step_pre, step, (entry, tail) = started[part]
@@ -987,11 +935,19 @@
             waits[part],
         )
         done.append((pair, act_grad, small))
-        sums.append(outer_quarters(*shared_by_four(pair), normed_four, cot_four))
+        out_rows = lax.dot_general(pair[0], cot_whole, contract_first, preferred_element_type=f32)
+        gate_rows = lax.dot_general(normed, pair[1], contract_first, preferred_element_type=f32)
+        half = gate_rows.shape[0] // 2
+        product = jnp.concatenate(
+            [out_rows, jnp.concatenate([gate_rows[:half], gate_rows[half:]], axis=1)]
+        ).astype(bf16)
+        waits[-1].append(product)
+        if part == 0:
+            share = lax.psum_scatter(product, "wide", scatter_dimension=0, tiled=True)
+            sums.append(lax.all_gather(share, "wide", axis=0, tiled=True))
+        else:
+            sums.append(lax.psum(product, "wide"))
     other_select_grad = swapped(select_grad, "narrow", 1)
-    place = (lax.axis_index("wide") & 3).astype(jnp.int32)[None]
-    sums = [shared_by_four(summed_above(piece, 1)) for piece in sums]
-    out_weight_grad = joined_out(place, *sums)
     scan_small = jnp.concatenate([small for _, _, small in done], axis=1)
     gated = jnp.concatenate([pair[0] for pair, _, _ in done], axis=1)
     gate_grad = jnp.concatenate([pair[1] for pair, _, _ in done], axis=1)
@@ -1035,19 +991,27 @@
     small = jnp.concatenate(
         [scan_small, conv_small, gain_part, jnp.zeros((spare, gain_part.shape[1]), f32)]
     )
-    near, far = shared_by_four(inner_grad)
-    inner_four = jnp.concatenate([near, far]).reshape(4 * rows, -1)
-    inner_piece = lax.dot_general(
-        normed_four.reshape(4 * rows, -1), inner_four, contract_first, preferred_element_type=f32
-    )
     small_piece = scattered(small, (1, 2))
-    groups = lax.axis_size("wide") // 4
-    last_piece = jnp.concatenate(
-        [x.reshape(groups, -1, x.shape[1]) for x in (inner_piece, small_piece)], axis=1
-    ).reshape(-1, inner_piece.shape[1])
-    inner_sum = shared_by_four(summed_above(last_piece, 2))
-    in_weight_grad, small_sum = joined_in(place, *sums, inner_sum)
-
+    near = swapped(inner_grad, "wide", 2)
+    wide_place = lax.axis_index("wide").astype(jnp.int32)
+    keep, sends = inner_quarter(
+        (wide_place >> 2 & 3)[None],
+        inner_grad,
+        near,
+        swapped(inner_grad, "wide", 1),
+        swapped(near, "wide", 1),
+        normed_four,
+        small_piece,
+    )
+    first_bits, *more_bits = group_bits(2)
+    held = keep
+    for n, flip in enumerate(flips(first_bits)[1:]):
+        held = held + swapped(sends[n], "wide", flip).astype(f32)
+    for bits in more_bits:
+        held = scattered(held, bits)
+    held = held.astype(bf16)
+    for bits in reversed(group_bits(2)):
+        held = gathered(held, bits)
     normed_mine, normed_other = narrow_halves(normed_part)
     row_sum = row_part + swapped(row_part, "narrow", 1)
     normed_sum = normed_mine + swapped(normed_other, "narrow", 1)
@@ -1057,6 +1021,20 @@
     ) * (row_sum / (2 * features))
     tokens_grad = (whole_grad + cotangent.astype(f32)).astype(bf16)
 
+    out_weight_grad = jnp.concatenate([total[:scan_width] for total in sums]).astype(f32)
+    near = swapped(held, "wide", 2)
+    quarters = (held, swapped(held, "wide", 1), near, swapped(near, "wide", 1))
+    results = []
+    for flip, quarter in enumerate(quarters):
+        results = joined(
+            (wide_place & 3)[None],
+            flip,
+            *sums,
+            quarter,
+            results,
+            [layer_out, tokens_grad, out_weight_grad] if flip == 2 else [],
+        )
+    in_weight_grad, small_sum = results
     scan_sum = small_sum[: scan_small.shape[0]]
     conv_sum = small_sum[scan_small.shape[0] : scan_small.shape[0] + conv_small.shape[0]]
     gain_row = scan_small.shape[0] + conv_small.shape[0]

time: 293 us -> 353 us (1.20)
  waiting for transfers between devices: 78.6 us -> 152 us
  starting transfers between devices: 78.4 us -> 53 us
  between operations: 1.45 us -> 14.2 us
  Pallas kernels: 78.9 us -> 72.6 us
    all_gather x0 -> x1, waiting for transfers between devices: none -> 42.9 us  [local(): sums.append(lax.all_gather(share, 'wide', axis=0, tiled=True))]
    ppermute x47 -> x30, starting transfers between devices: 59.5 us -> 32.6 us  [swapped(): return lax.ppermute(array, axis, [(i, i ^ bit) for i in range(peers)])]
    psum x0 -> x1, waiting for transfers between devices: none -> 20.8 us  [local(): sums.append(lax.psum(product, 'wide'))]
    pallas_call x4 -> x5, Pallas kernels: 21.2 us -> 14.4 us  [the longest x4 11 us: joined(): pl.pallas_call(join_kernel, grid_spec=pltpu.PrefetchScalarGridSpec(num_sc...]
    ppermute x47 -> x30, waiting for transfers between devices: 76.4 us -> 83 us  [swapped(): return lax.ppermute(array, axis, [(i, i ^ bit) for i in range(peers)])]
    dot_general x1 -> x4, matrix products: 0.7 us -> 4.71 us  [the longest x2 2.82 us: local(): lax.dot_general(pair[0], cot_whole, contract_first, preferred_element_typ...]
    another operation x9 -> x0, other arithmetic: 3.87 us -> none  [shared_by_four(): near = jnp.stack([array, swapped(array, 'wide', 2)])]
    convert_element_type x3 -> x2, other arithmetic: 0.15 us -> 3.72 us  [the longest x1 2.46 us: local(): jnp.concatenate([total[:scan_width] for total in sums]).astype(f32)]
  transfers between devices with their start and end apart: 54 -> 40, of which waited for: 17 -> 19; matrix products, arithmetic and copies ran while one was open for 16% -> 13% of each run, Pallas kernels for 22% -> 13%
where the time goes in v5:
time: 353 us; the launch traced here: 351 us
  waiting for transfers between devices  152 us (43%)
  Pallas kernels  72.6 us (21%)
  starting transfers between devices  53 us (15%)
  other arithmetic  23.9 us (7%)
  local copies, waits for them, and re-layouts  19.3 us (5%)
  matrix products  15.9 us (5%)
  between operations  14.2 us (4%)
    ppermute x30, waiting for transfers between devices, swapped(): return lax.ppermute(array, axis, [(i, i ^ bit) for i in range(peers)])  83 us
    pallas_call x7, Pallas kernels, call(): pl.pallas_call(kernel, grid=(width // scan_width,), in_specs=in_specs, ou...  54.5 us
    all_gather x1, waiting for transfers between devices, local(): sums.append(lax.all_gather(share, 'wide', axis=0, tiled=True))  42.9 us
    ppermute x30, starting transfers between devices, swapped(): return lax.ppermute(array, axis, [(i, i ^ bit) for i in range(peers)])  32.6 us
    psum x1, waiting for transfers between devices, local(): sums.append(lax.psum(product, 'wide'))  20.8 us
    ppermute x6, starting transfers between devices, passed_along(): return lax.ppermute(array, axis, pairs)  14.4 us
    pallas_call x4, Pallas kernels, joined(): pl.pallas_call(join_kernel, grid_spec=pltpu.PrefetchScalarGridSpec(num_sc...  11 us
  transfers between devices with their start and end apart: 40, of which 19 were waited for; matrix products, arithmetic and copies ran while one was open for 13% of the time, Pallas kernels for 13%

profile of v5, /device:TPU:0, one launch (start us, length us, event | category | flops | bytes accessed | tf_op | source)
XLA Modules:
  0.0 351.0 jit_solution(6151571582238769069)
XLA Ops:
  7.2 1.5 edge_rows.1
  8.7 2.3 collective-permute-start.1
  11.1 5.6 %collective-permute-start.2 = (bf16[16,512]{1,0:T(8,128)(2,1)}, bf16[16,512]{1,0:T(8,128)(2,1)S(1)}, u32[]{:S(2)}, u32[]{:S(2)}) collective-permute-start(bf16[16,512]{1,0:T(8,128)(2,1)} %edge_rows.1), channel_id=1, source_target_pairs={{0,3},{1,2},{2,5},{3,4},{4,7},{5,6},{6,9},{7,8},{8,11},{9,10},{10,... | collective-permute-start | bytes 49160 | tf_op jit(solution)/shard_map/ppermute | solution.py:50
  17.3 1.5 collective-permute-start.4
  21.0 1.5 compare_convert_fusion
  23.4 2.8 collective-permute-done.other_ref
  26.9 2.2 normalized.1
  29.1 4.9 %fusion.7.inner_ref.gate_ref = bf16[2,272,1024]{2,1,0:T(8,128)(2,1)} fusion(bf16[1024,2,1024]{2,1,0:T(2,128)(2,1)} %param.15, bf16[272,1024]{1,0:T(8,128)(2,1)} %get-tuple-element.48), kind=kOutput, calls=%fused_computation.12 | convolution fusion | flops 1141407744 | bytes 5865472 | tf_op jit(solution)/shard_map/td,dce->cte/dot_general | solution.py:883
  34.0 3.6 %convolve.1 = (f32[256,1024]{1,0:T(8,128)}, bf16[256,1024]{1,0:T(8,128)(2,1)}, f32[96,256]{1,0:T(8,128)}) custom-call(bf16[2,272,1024]{2,1,0:T(8,128)(2,1)} %fusion.7.inner_ref.gate_ref, f32[4,1024]{1,0:T(4,128)} %conv_weight_ref.5, f32[1,1024]{1,0:T(1,128)} %bitcast.102, bf16[96,1024]{1,0:T(8,128)(2,1)} %select_ref.5, f32[256,8]{1,0:T(8,128)} %copy.43.mask_ref), custom_call_target="tpu_custom_call" | custom-call | flops 4000000000 | bytes 1339392 | tf_op jit(solution)/shard_map/convolve/pallas_call | solution.py:129
  38.1 1.7 fusion.33.gated_grad_ref
  39.8 2.6 collective-permute-done.3.other_ref
  43.0 6.6 %scan_ends.2 = (f32[256,512]{1,0:T(8,128)}, f32[256,512]{1,0:T(8,128)}, f32[40,512]{1,0:T(8,128)}) custom-call(f32[96,256]{1,0:T(8,128)} %get-tuple-element.49.selected_ref, f32[96,256]{1,0:T(8,128)} %copy-done.20, bf16[64,1024]{1,0:T(8,128)(2,1)} %step_weight_ref.7, f32[1,1024]{1,0:T(1,128)} %bitcast.103, bf16[256,1024]{1,0:T(8,128)(2,1)} %get-tuple-element.50.act_ref, ...), custom_call_target="tpu_custom_call" | custom-call | flops 5000000000 | bytes 3092480 | tf_op jit(solution)/shard_map/scan_ends/pallas_call | solution.py:129
  49.6 6.7 %scan_ends.3 = (f32[256,512]{1,0:T(8,128)}, f32[256,512]{1,0:T(8,128)}, f32[40,512]{1,0:T(8,128)}) custom-call(f32[96,256]{1,0:T(8,128)} %get-tuple-element.49.selected_ref, f32[96,256]{1,0:T(8,128)} %copy-done.20, bf16[64,1024]{1,0:T(8,128)(2,1)} %step_weight_ref.7, f32[1,1024]{1,0:T(1,128)} %bitcast.104, bf16[256,1024]{1,0:T(8,128)(2,1)} %get-tuple-element.50.act_ref, ...), custom_call_target="tpu_custom_call" | custom-call | flops 5000000000 | bytes 3092480 | tf_op jit(solution)/shard_map/scan_ends/pallas_call | solution.py:129
  56.9 1.6 collective-permute-start.6
  58.5 2.9 collective-permute-done.6
  62.9 1.6 collective-permute-start.10
  64.6 3.5 collective-permute-start.7
  69.4 4.5 %collective-permute-start.11 = (f32[16,512]{1,0:T(8,128)S(1)}, f32[16,512]{1,0:T(8,128)S(1)}, u32[]{:S(2)}, u32[]{:S(2)}) collective-permute-start(f32[16,512]{1,0:T(8,128)S(1)} %get-tuple-element.149), channel_id=1, source_target_pairs={{0,8},{2,10},{4,12},{6,14},{8,16},{10,18},{12,20},{14,22},{16,24},... | collective-permute-start | bytes 98312 | tf_op jit(solution)/shard_map/ppermute | solution.py:27
  76.1 3.6 %collective-permute-done.12 = f32[16,512]{1,0:T(8,128)S(1)} collective-permute-done((f32[16,512]{1,0:T(8,128)S(1)}, f32[16,512]{1,0:T(8,128)S(1)}, u32[]{:S(2)}, u32[]{:S(2)}) %collective-permute-start.12) | collective-permute-done | bytes 32800 | tf_op jit(solution)/shard_map/ppermute | solution.py:27
  81.1 15.4 %scan_full.2 = (bf16[2,256,512]{2,1,0:T(8,128)(2,1)}, f32[256,512]{1,0:T(8,128)}, f32[96,256]{1,0:T(8,128)}, f32[96,512]{1,0:T(8,128)}) custom-call(f32[96,256]{1,0:T(8,128)} %get-tuple-element.49.selected_ref, f32[96,256]{1,0:T(8,128)} %copy-done.20, f32[256,512]{1,0:T(8,128)} %get-tuple-element.51.step_pre_ref, f32[256,512]{1,0:T(8,128)} %get-tuple-element.52.step_ref, ...), custom_call_target="tpu_custom_call" | custom-call | flops 12999999488 | bytes 4337664 | tf_op jit(solution)/shard_map/scan_full/pallas_call | solution.py:129
  99.4 1.6 maximum_maximum_fusion.rest_1_
  101.8 1.7 collective-permute-start.15
  104.4 3.2 collective-permute-done.13
  107.6 1.9 pad_maximum_fusion.2.rest_0_.normed_ref
  109.4 15.5 %scan_full.3 = (bf16[2,256,512]{2,1,0:T(8,128)(2,1)}, f32[256,512]{1,0:T(8,128)}, f32[96,256]{1,0:T(8,128)}, f32[96,512]{1,0:T(8,128)}) custom-call(f32[96,256]{1,0:T(8,128)} %get-tuple-element.49.selected_ref, f32[96,256]{1,0:T(8,128)} %copy-done.20, f32[256,512]{1,0:T(8,128)} %get-tuple-element.56.step_pre_ref, f32[256,512]{1,0:T(8,128)} %get-tuple-element.57.step_ref, ...), custom_call_target="tpu_custom_call" | custom-call | flops 12999999488 | bytes 6926336 | tf_op jit(solution)/shard_map/scan_full/pallas_call | solution.py:129
  125.5 1.8 slice_bitcast_fusion
  129.2 1.6 maximum_maximum_fusion.1
  131.1 3.3 convolve_grad.2
  135.2 3.5 convolve_grad.3
  141.6 1.7 collective-permute-done.18
  143.3 1.8 fusion.28.own_ref
  145.1 2.5 collective-permute-start.21
  149.1 2.9 fusion.15
  152.0 9.2 %collective-permute-done.21.near_ref = bf16[256,1024]{1,0:T(8,128)(2,1)} collective-permute-done((bf16[256,1024]{1,0:T(8,128)(2,1)}, bf16[256,1024]{1,0:T(8,128)(2,1)}, u32[]{:S(2)}, u32[]{:S(2)}) %collective-permute-start.21) | collective-permute-done | bytes 524320 | tf_op jit(solution)/shard_map/ppermute | solution.py:32
  165.1 1.7 collective-permute-start.25
  167.0 4.7 %collective-permute-done.25 = bf16[64,1024]{1,0:T(8,128)(2,1)} collective-permute-done((bf16[64,1024]{1,0:T(8,128)(2,1)}, bf16[64,1024]{1,0:T(8,128)(2,1)}, u32[]{:S(2)}, u32[]{:S(2)}) %collective-permute-start.25) | collective-permute-done | bytes 131104 | tf_op jit(solution)/shard_map/ppermute | solution.py:32
  171.7 3.1 collective-permute-done.26
  174.8 1.9 convert_add_fusion.1.small_ref
  176.7 3.4 inner_quarter.1
  180.1 1.9 slice_bitcast_fusion.6
  182.0 1.9 collective-permute-start.27
  184.4 2.0 collective-permute-start.29
  186.3 8.7 %collective-permute-done.27 = bf16[80,1024]{1,0:T(8,128)(2,1)} collective-permute-done((bf16[80,1024]{1,0:T(8,128)(2,1)}, bf16[80,1024]{1,0:T(8,128)(2,1)}, u32[]{:S(2)}, u32[]{:S(2)}) %collective-permute-start.27) | collective-permute-done | bytes 163872 | tf_op jit(solution)/shard_map/ppermute | solution.py:32
  195.0 3.5 %collective-permute-done.28 = bf16[80,1024]{1,0:T(8,128)(2,1)} collective-permute-done((bf16[80,1024]{1,0:T(8,128)(2,1)}, bf16[80,1024]{1,0:T(8,128)(2,1)}, u32[]{:S(2)}, u32[]{:S(2)}) %collective-permute-start.28) | collective-permute-done | bytes 163872 | tf_op jit(solution)/shard_map/ppermute | solution.py:32
  198.5 4.2 %collective-permute-done.29 = bf16[80,1024]{1,0:T(8,128)(2,1)} collective-permute-done((bf16[80,1024]{1,0:T(8,128)(2,1)}, bf16[80,1024]{1,0:T(8,128)(2,1)}, u32[]{:S(2)}, u32[]{:S(2)}) %collective-permute-start.29) | collective-permute-done | bytes 163872 | tf_op jit(solution)/shard_map/ppermute | solution.py:32
  204.0 4.8 %collective-permute-start.32 = (bf16[80,1024]{1,0:T(8,128)(2,1)S(1)}, bf16[80,1024]{1,0:T(8,128)(2,1)S(1)}, u32[]{:S(2)}, u32[]{:S(2)}) collective-permute-start(bf16[80,1024]{1,0:T(8,128)(2,1)S(1)} %add_convert_fusion), channel_id=1, source_target_pairs={{0,8},{2,10},{4,12},{6,14},{8,0},{10,2},{12,4},{14,6},{16,24},{18,... | collective-permute-start | bytes 491528 | tf_op jit(solution)/shard_map/ppermute | solution.py:32
  208.8 1.7 fusion.29
  210.5 2.2 collective-permute-start.30
  212.6 1.7 collective-permute-done.32
  214.4 7.1 %collective-permute-done.30 = bf16[80,1024]{1,0:T(8,128)(2,1)S(1)} collective-permute-done((bf16[80,1024]{1,0:T(8,128)(2,1)S(1)}, bf16[80,1024]{1,0:T(8,128)(2,1)S(1)}, u32[]{:S(2)}, u32[]{:S(2)}) %collective-permute-start.30) | collective-permute-done | bytes 163872 | tf_op jit(solution)/shard_map/ppermute | solution.py:32
  221.5 8.4 %collective-permute-done.31 = bf16[80,1024]{1,0:T(8,128)(2,1)S(1)} collective-permute-done((bf16[80,1024]{1,0:T(8,128)(2,1)S(1)}, bf16[80,1024]{1,0:T(8,128)(2,1)S(1)}, u32[]{:S(2)}, u32[]{:S(2)}) %collective-permute-start.31) | collective-permute-done | bytes 163872 | tf_op jit(solution)/shard_map/ppermute | solution.py:32
  235.4 14.3 %collective-permute-done.33.inner_ref = bf16[320,1024]{1,0:T(8,128)(2,1)} collective-permute-done((bf16[320,1024]{1,0:T(8,128)(2,1)}, bf16[320,1024]{1,0:T(8,128)(2,1)}, u32[]{:S(2)}, u32[]{:S(2)}) %collective-permute-start.33) | collective-permute-done | bytes 655392 | tf_op jit(solution)/shard_map/ppermute | solution.py:32
  249.7 6.5 %collective-permute-done.20 = f32[256,1]{0,1:T(1,128)S(1)} collective-permute-done((f32[256,1]{0,1:T(1,128)S(1)}, f32[256,1]{0,1:T(1,128)S(1)}, u32[]{:S(2)}, u32[]{:S(2)}) %collective-permute-start.20) | collective-permute-done | bytes 1056 | tf_op jit(solution)/shard_map/ppermute | solution.py:32
  257.3 20.8 %all-reduce.3.cloned.1.call-done.second_ref = bf16[1024,1024]{1,0:T(8,128)(2,1)} async-done(((bf16[1024,1024]{1,0:T(8,128)(2,1)}), bf16[1024,1024]{1,0:T(8,128)(2,1)}) %all-reduce.3.cloned.1.call-update) | async-done | bytes 2097168 | tf_op jit(solution)/shard_map/psum | solution.py:949
  278.1 42.9 %all-gather.2.cloned.1.call-done.first_ref = bf16[1024,1024]{1,0:T(8,128)(2,1)} async-done(((bf16[64,1024]{1,0:T(8,128)(2,1)}), bf16[1024,1024]{1,0:T(8,128)(2,1)}) %all-gather.2.cloned.1.call-update) | async-done | bytes 2097168 | tf_op jit(solution)/shard_map/all_gather | solution.py:947
  321.0 2.7 joined.4
  323.7 2.9 joined.5
  326.6 2.5 maximum_convert_fusion.rest_4_
  329.1 2.7 joined.6
  331.8 2.7 joined.7
  335.3 1.5 collective-permute-start.36
  336.8 1.8 slice.246
  338.5 1.7 slice.247
  340.2 1.5 slice.249
  (148 shorter events, 40.8 us)
Async XLA Ops:
  7.2 30.9 %copy-start = (bf16[1024,1024]{1,0:T(8,128)(2,1)S(1)}, bf16[1024,1024]{1,0:T(8,128)(2,1)}, u32[]{:S(2)}) copy-start(bf16[1024,1024]{1,0:T(8,128)(2,1)} %param.23) | copy-start | bytes 6291460
  7.2 154.8 %reduce-scatter.2.cloned.1.call-start = ((), (), s32[]{:S(2)}) async-start(), calls=%async_computation.1 | async-start | bytes 2228224 | tf_op jit(solution)/shard_map/reduce_scatter | solution.py:946
  8.7 14.7 %collective-permute-start.1 = (bf16[16,512]{1,0:T(8,128)(2,1)}, bf16[16,512]{1,0:T(8,128)(2,1)S(1)}, u32[]{:S(2)}, u32[]{:S(2)}) collective-permute-start(bf16[16,512]{1,0:T(8,128)(2,1)} %edge_rows.1), channel_id=1, source_target_pairs={{0,2},{2,4},{4,6},{6,8},{8,10},{10,12},{12,14},{14,16},{16,18},{18... | collective-permute-start | bytes 49160 | tf_op jit(solution)/shard_map/ppermute | solution.py:27
  11.1 12.3 %collective-permute-start.2 = (bf16[16,512]{1,0:T(8,128)(2,1)}, bf16[16,512]{1,0:T(8,128)(2,1)S(1)}, u32[]{:S(2)}, u32[]{:S(2)}) collective-permute-start(bf16[16,512]{1,0:T(8,128)(2,1)} %edge_rows.1), channel_id=1, source_target_pairs={{0,3},{1,2},{2,5},{3,4},{4,7},{5,6},{6,9},{7,8},{8,11},{9,10},{10,... | collective-permute-start | bytes 49160 | tf_op jit(solution)/shard_map/ppermute | solution.py:50
  16.7 9.5 %collective-permute-start = (bf16[256,512]{1,0:T(8,128)(2,1)}, bf16[256,512]{1,0:T(8,128)(2,1)S(1)}, u32[]{:S(2)}, u32[]{:S(2)}) collective-permute-start(bf16[256,512]{1,0:T(8,128)(2,1)} %own_ref.1), channel_id=1, source_target_pairs={{0,1},{1,0},{2,3},{3,2},{4,5},{5,4},{6,7},{7,6},{8,9},{9,8},{10,11... | collective-permute-start | bytes 786440 | tf_op jit(solution)/shard_map/ppermute | solution.py:32
  17.3 20.8 %collective-permute-start.4 = (bf16[256,512]{1,0:T(8,128)(2,1)}, bf16[256,512]{1,0:T(8,128)(2,1)S(1)}, u32[]{:S(2)}, u32[]{:S(2)}) collective-permute-start(bf16[256,512]{1,0:T(8,128)(2,1)} %param.25), channel_id=1, source_target_pairs={{0,1},{1,0},{2,3},{3,2},{4,5},{5,4},{6,7},{7,6},{8,9},{9,8},{10,11... | collective-permute-start | bytes 786440 | tf_op jit(solution)/shard_map/ppermute | solution.py:32
  23.4 2.8 copy-start.15
  23.4 2.8 copy-start.16
  26.2 0.7 copy-start.10
  34.0 4.1 %copy-start.3 = (bf16[256,512]{1,0:T(8,128)(2,1)S(1)}, bf16[256,512]{1,0:T(8,128)(2,1)}, u32[]{:S(2)}) copy-start(bf16[256,512]{1,0:T(8,128)(2,1)} %param.25) | copy-start | bytes 786436
  37.5 4.8 %collective-permute-start.3 = (f32[96,256]{1,0:T(8,128)}, f32[96,256]{1,0:T(8,128)S(1)}, u32[]{:S(2)}, u32[]{:S(2)}) collective-permute-start(f32[96,256]{1,0:T(8,128)} %get-tuple-element.49.selected_ref), channel_id=1, source_target_pairs={{0,1},{1,0},{2,3},{3,2},{4,5},{5,4},{6,7},{7,6},{8,9},{9,8},{10,11... | collective-permute-start | bytes 294920 | tf_op jit(solution)/shard_map/ppermute | solution.py:32
  42.4 0.6 copy-start.20
  49.6 7.1 %copy-start.13 = (f32[40,512]{1,0:T(8,128)S(1)}, f32[40,512]{1,0:T(8,128)}, u32[]{:S(2)}) copy-start(f32[40,512]{1,0:T(8,128)} %get-tuple-element.53) | copy-start | bytes 245764
  49.6 7.1 %collective-permute-start.5 = (f32[40,512]{1,0:T(8,128)}, f32[40,512]{1,0:T(8,128)S(1)}, u32[]{:S(2)}, u32[]{:S(2)}) collective-permute-start(f32[40,512]{1,0:T(8,128)} %get-tuple-element.53), channel_id=1, source_target_pairs={{0,2},{2,0},{4,6},{6,4},{8,10},{10,8},{12,14},{14,12},{16,18},{18,... | collective-permute-start | bytes 245768 | tf_op jit(solution)/shard_map/ppermute | solution.py:32
  56.3 2.2 collective-permute-start.9
  56.9 4.5 %collective-permute-start.6 = (f32[40,512]{1,0:T(8,128)S(1)}, f32[40,512]{1,0:T(8,128)S(1)}, u32[]{:S(2)}, u32[]{:S(2)}) collective-permute-start(f32[40,512]{1,0:T(8,128)S(1)} %pad_maximum_fusion.8), channel_id=1, source_target_pairs={{0,4},{2,6},{4,0},{6,2},{8,12},{10,14},{12,8},{14,10},{16,20},{18,... | collective-permute-start | bytes 245768 | tf_op jit(solution)/shard_map/ppermute | solution.py:32
  62.9 6.4 %collective-permute-start.10 = (f32[40,512]{1,0:T(8,128)S(1)}, f32[40,512]{1,0:T(8,128)S(1)}, u32[]{:S(2)}, u32[]{:S(2)}) collective-permute-start(f32[40,512]{1,0:T(8,128)S(1)} %pad_maximum_fusion.9), channel_id=1, source_target_pairs={{0,4},{2,6},{4,0},{6,2},{8,12},{10,14},{12,8},{14,10},{16,20},{18,... | collective-permute-start | bytes 245768 | tf_op jit(solution)/shard_map/ppermute | solution.py:32
  64.6 10.9 %collective-permute-start.7 = (f32[16,512]{1,0:T(8,128)S(1)}, f32[16,512]{1,0:T(8,128)S(1)}, u32[]{:S(2)}, u32[]{:S(2)}) collective-permute-start(f32[16,512]{1,0:T(8,128)S(1)} %get-tuple-element.147), channel_id=1, source_target_pairs={{0,8},{2,10},{4,12},{6,14},{8,16},{10,18},{12,20},{14,22},{16,24},... | collective-permute-start | bytes 98312 | tf_op jit(solution)/shard_map/ppermute | solution.py:27
  68.0 7.4 %collective-permute-start.8 = (f32[16,512]{1,0:T(8,128)S(1)}, f32[16,512]{1,0:T(8,128)S(1)}, u32[]{:S(2)}, u32[]{:S(2)}) collective-permute-start(f32[16,512]{1,0:T(8,128)S(1)} %get-tuple-element.146), channel_id=1, source_target_pairs={{8,0},{10,2},{12,4},{14,6},{16,8},{18,10},{20,12},{22,14},{24,16},... | collective-permute-start | bytes 98312 | tf_op jit(solution)/shard_map/ppermute | solution.py:27
  69.4 6.7 %collective-permute-start.11 = (f32[16,512]{1,0:T(8,128)S(1)}, f32[16,512]{1,0:T(8,128)S(1)}, u32[]{:S(2)}, u32[]{:S(2)}) collective-permute-start(f32[16,512]{1,0:T(8,128)S(1)} %get-tuple-element.149), channel_id=1, source_target_pairs={{0,8},{2,10},{4,12},{6,14},{8,16},{10,18},{12,20},{14,22},{16,24},... | collective-permute-start | bytes 98312 | tf_op jit(solution)/shard_map/ppermute | solution.py:27
  74.0 5.8 %collective-permute-start.12 = (f32[16,512]{1,0:T(8,128)S(1)}, f32[16,512]{1,0:T(8,128)S(1)}, u32[]{:S(2)}, u32[]{:S(2)}) collective-permute-start(f32[16,512]{1,0:T(8,128)S(1)} %get-tuple-element.148), channel_id=1, source_target_pairs={{8,0},{10,2},{12,4},{14,6},{16,8},{18,10},{20,12},{22,14},{24,16},... | collective-permute-start | bytes 98312 | tf_op jit(solution)/shard_map/ppermute | solution.py:27
  81.1 15.4 %copy-start.8 = (bf16[272,1024]{1,0:T(8,128)(2,1)S(1)}, bf16[272,1024]{1,0:T(8,128)(2,1)}, u32[]{:S(2)}) copy-start(bf16[272,1024]{1,0:T(8,128)(2,1)} %get-tuple-element.48) | copy-start | bytes 1671172
  101.0 2.4 copy-start.17
  101.0 3.2 copy-start.12
  101.0 177.1 %all-reduce.3.cloned.1.call-start = ((), (), s32[]{:S(2)}) async-start(), calls=%async_computation.3 | async-start | bytes 4194304 | tf_op jit(solution)/shard_map/psum | solution.py:949
  101.2 6.3 %collective-permute-start.13 = (bf16[256,256]{1,0:T(8,128)(2,1)S(1)}, bf16[256,256]{1,0:T(8,128)(2,1)S(1)}, u32[]{:S(2)}, u32[]{:S(2)}) collective-permute-start(bf16[256,256]{1,0:T(8,128)(2,1)S(1)} %get-tuple-element.122), channel_id=1, source_target_pairs={{0,4},{2,6},{4,0},{6,2},{8,12},{10,14},{12,8},{14,10},{16,20},{18,... | collective-permute-start | bytes 393224 | tf_op jit(solution)/shard_map/ppermute | solution.py:32
  101.8 5.8 %collective-permute-start.14 = (bf16[256,256]{1,0:T(8,128)(2,1)S(1)}, bf16[256,256]{1,0:T(8,128)(2,1)}, u32[]{:S(2)}, u32[]{:S(2)}) collective-permute-start(bf16[256,256]{1,0:T(8,128)(2,1)S(1)} %get-tuple-element.121), channel_id=1, source_target_pairs={{0,2},{2,0},{4,6},{6,4},{8,10},{10,8},{12,14},{14,12},{16,18},{18,... | collective-permute-start | bytes 393224 | tf_op jit(solution)/shard_map/ppermute | solution.py:32
  101.8 5.8 %collective-permute-start.15 = (bf16[256,256]{1,0:T(8,128)(2,1)S(1)}, bf16[256,256]{1,0:T(8,128)(2,1)}, u32[]{:S(2)}, u32[]{:S(2)}) collective-permute-start(bf16[256,256]{1,0:T(8,128)(2,1)S(1)} %get-tuple-element.120), channel_id=1, source_target_pairs={{0,6},{2,4},{4,2},{6,0},{8,14},{10,12},{12,10},{14,8},{16,22},{18,... | collective-permute-start | bytes 393224 | tf_op jit(solution)/shard_map/ppermute | solution.py:32
  124.9 3.7 %copy-start.7 = (bf16[2,256,512]{2,1,0:T(8,128)(2,1)S(1)}, bf16[2,256,512]{2,1,0:T(8,128)(2,1)}, u32[]{:S(2)}) copy-start(bf16[2,256,512]{2,1,0:T(8,128)(2,1)} %get-tuple-element.59) | copy-start | bytes 1572868
  124.9 3.7 %copy-start.9 = (bf16[272,1024]{1,0:T(8,128)(2,1)S(1)}, bf16[272,1024]{1,0:T(8,128)(2,1)}, u32[]{:S(2)}) copy-start(bf16[272,1024]{1,0:T(8,128)(2,1)} %get-tuple-element.48) | copy-start | bytes 1671172
  124.9 6.2 %collective-permute-start.17 = (f32[96,256]{1,0:T(8,128)}, f32[96,256]{1,0:T(8,128)}, u32[]{:S(2)}, u32[]{:S(2)}) collective-permute-start(f32[96,256]{1,0:T(8,128)} %get-tuple-element.61.select_grad_ref), channel_id=1, source_target_pairs={{0,1},{1,0},{2,3},{3,2},{4,5},{5,4},{6,7},{7,6},{8,9},{9,8},{10,11... | collective-permute-start | bytes 294920 | tf_op jit(solution)/shard_map/ppermute | solution.py:32
  130.8 190.2 %all-gather.2.cloned.1.call-start = ((), (), s32[]{:S(2)}) async-start(), calls=%async_computation.2 | async-start | bytes 2228224 | tf_op jit(solution)/shard_map/all_gather | solution.py:947
  135.2 5.6 %copy-start.6 = (bf16[2,256,512]{2,1,0:T(8,128)(2,1)S(1)}, bf16[2,256,512]{2,1,0:T(8,128)(2,1)}, u32[]{:S(2)}) copy-start(bf16[2,256,512]{2,1,0:T(8,128)(2,1)} %get-tuple-element.55) | copy-start | bytes 1572868
  135.2 8.1 %copy-start.11 = (bf16[256,512]{1,0:T(8,128)(2,1)S(1)}, bf16[256,512]{1,0:T(8,128)(2,1)}, u32[]{:S(2)}) copy-start(bf16[256,512]{1,0:T(8,128)(2,1)} %get-tuple-element.64) | copy-start | bytes 786436
  135.2 13.9 %copy-start.18 = (bf16[1024,2,1024]{2,1,0:T(2,128)(2,1)S(1)}, bf16[1024,2,1024]{2,1,0:T(2,128)(2,1)}, u32[]{:S(2)}) copy-start(bf16[1024,2,1024]{2,1,0:T(2,128)(2,1)} %param.15) | copy-start | bytes 12582916
  138.7 9.0 %copy-start.5 = (bf16[256,512]{1,0:T(8,128)(2,1)S(1)}, bf16[256,512]{1,0:T(8,128)(2,1)}, u32[]{:S(2)}) copy-start(bf16[256,512]{1,0:T(8,128)(2,1)} %get-tuple-element.117) | copy-start | bytes 786436
  138.7 10.4 %copy-start.14 = (f32[1024]{0:T(1024)S(1)}, f32[1024]{0:T(1024)}, u32[]{:S(2)}) copy-start(f32[1024]{0:T(1024)} %param.14) | copy-start | bytes 12292
  138.7 10.4 %copy-start.19 = (bf16[272,1024]{1,0:T(8,128)(2,1)S(1)}, bf16[272,1024]{1,0:T(8,128)(2,1)}, u32[]{:S(2)}) copy-start(bf16[272,1024]{1,0:T(8,128)(2,1)} %get-tuple-element.69) | copy-start | bytes 1671172
  139.5 3.7 %collective-permute-start.18 = (f32[8,1024]{1,0:T(8,128)S(1)}, f32[8,1024]{1,0:T(8,128)S(1)}, u32[]{:S(2)}, u32[]{:S(2)}) collective-permute-start(f32[8,1024]{1,0:T(8,128)S(1)} %slice.270), channel_id=1, source_target_pairs={{2,0},{4,2},{6,4},{8,6},{10,8},{12,10},{14,12},{16,14},{18,16},{20... | collective-permute-start | bytes 98312 | tf_op jit(solution)/shard_map/ppermute | solution.py:27
  145.1 16.1 %collective-permute-start.21 = (bf16[256,1024]{1,0:T(8,128)(2,1)}, bf16[256,1024]{1,0:T(8,128)(2,1)}, u32[]{:S(2)}, u32[]{:S(2)}) collective-permute-start(bf16[256,1024]{1,0:T(8,128)(2,1)} %fusion.28.own_ref), channel_id=1, source_target_pairs={{0,4},{2,6},{4,0},{6,2},{8,12},{10,14},{12,8},{14,10},{16,20},{18,... | collective-permute-start | bytes 1572872 | tf_op jit(solution)/shard_map/ppermute | solution.py:32
  147.7 29.0 %collective-permute-start.22 = (bf16[256,1024]{1,0:T(8,128)(2,1)}, bf16[256,1024]{1,0:T(8,128)(2,1)}, u32[]{:S(2)}, u32[]{:S(2)}) collective-permute-start(bf16[256,1024]{1,0:T(8,128)(2,1)} %fusion.28.own_ref), channel_id=1, source_target_pairs={{0,2},{2,0},{4,6},{6,4},{8,10},{10,8},{12,14},{14,12},{16,18},{18,... | collective-permute-start | bytes 1572872 | tf_op jit(solution)/shard_map/ppermute | solution.py:32
  161.2 15.5 %collective-permute-start.23 = (bf16[256,1024]{1,0:T(8,128)(2,1)}, bf16[256,1024]{1,0:T(8,128)(2,1)}, u32[]{:S(2)}, u32[]{:S(2)}) collective-permute-start(bf16[256,1024]{1,0:T(8,128)(2,1)} %collective-permute-done.21.near_ref), channel_id=1, source_target_pairs={{0,2},{2,0},{4,6},{6,4},{8,10},{10,8},{12,14},{14,12},{16,18},{18,... | collective-permute-start | bytes 1572872 | tf_op jit(solution)/shard_map/ppermute | solution.py:32
  163.4 1.0 copy-start.1
  165.1 1.9 collective-permute-start.24
  165.1 6.6 %collective-permute-start.25 = (bf16[64,1024]{1,0:T(8,128)(2,1)}, bf16[64,1024]{1,0:T(8,128)(2,1)}, u32[]{:S(2)}, u32[]{:S(2)}) collective-permute-start(bf16[64,1024]{1,0:T(8,128)(2,1)} %get-tuple-element.108), channel_id=1, source_target_pairs={{0,4},{2,6},{4,0},{6,2},{8,12},{10,14},{12,8},{14,10},{16,20},{18,... | collective-permute-start | bytes 393224 | tf_op jit(solution)/shard_map/ppermute | solution.py:32
  166.9 8.0 %collective-permute-start.26 = (bf16[64,1024]{1,0:T(8,128)(2,1)}, bf16[64,1024]{1,0:T(8,128)(2,1)}, u32[]{:S(2)}, u32[]{:S(2)}) collective-permute-start(bf16[64,1024]{1,0:T(8,128)(2,1)} %get-tuple-element.107), channel_id=1, source_target_pairs={{0,6},{2,4},{4,2},{6,0},{8,14},{10,12},{12,10},{14,8},{16,22},{18,... | collective-permute-start | bytes 393224 | tf_op jit(solution)/shard_map/ppermute | solution.py:32
  182.0 13.1 %collective-permute-start.27 = (bf16[80,1024]{1,0:T(8,128)(2,1)}, bf16[80,1024]{1,0:T(8,128)(2,1)}, u32[]{:S(2)}, u32[]{:S(2)}) collective-permute-start(bf16[80,1024]{1,0:T(8,128)(2,1)} %get-tuple-element.125), channel_id=1, source_target_pairs={{0,8},{2,10},{4,12},{6,14},{8,0},{10,2},{12,4},{14,6},{16,24},{18,... | collective-permute-start | bytes 491528 | tf_op jit(solution)/shard_map/ppermute | solution.py:32
  183.9 14.7 %collective-permute-start.28 = (bf16[80,1024]{1,0:T(8,128)(2,1)}, bf16[80,1024]{1,0:T(8,128)(2,1)}, u32[]{:S(2)}, u32[]{:S(2)}) collective-permute-start(bf16[80,1024]{1,0:T(8,128)(2,1)} %get-tuple-element.127), channel_id=1, source_target_pairs={{0,16},{2,18},{4,20},{6,22},{8,24},{10,26},{12,28},{14,30},{16,0},... | collective-permute-start | bytes 491528 | tf_op jit(solution)/shard_map/ppermute | solution.py:32
  184.4 18.4 %collective-permute-start.29 = (bf16[80,1024]{1,0:T(8,128)(2,1)}, bf16[80,1024]{1,0:T(8,128)(2,1)}, u32[]{:S(2)}, u32[]{:S(2)}) collective-permute-start(bf16[80,1024]{1,0:T(8,128)(2,1)} %get-tuple-element.126), channel_id=1, source_target_pairs={{0,24},{2,26},{4,28},{6,30},{8,16},{10,18},{12,20},{14,22},{16,8},... | collective-permute-start | bytes 491528 | tf_op jit(solution)/shard_map/ppermute | solution.py:32
  204.0 10.3 %collective-permute-start.32 = (bf16[80,1024]{1,0:T(8,128)(2,1)S(1)}, bf16[80,1024]{1,0:T(8,128)(2,1)S(1)}, u32[]{:S(2)}, u32[]{:S(2)}) collective-permute-start(bf16[80,1024]{1,0:T(8,128)(2,1)S(1)} %add_convert_fusion), channel_id=1, source_target_pairs={{0,8},{2,10},{4,12},{6,14},{8,0},{10,2},{12,4},{14,6},{16,24},{18,... | collective-permute-start | bytes 491528 | tf_op jit(solution)/shard_map/ppermute | solution.py:32
  210.5 11.0 %collective-permute-start.30 = (bf16[80,1024]{1,0:T(8,128)(2,1)S(1)}, bf16[80,1024]{1,0:T(8,128)(2,1)S(1)}, u32[]{:S(2)}, u32[]{:S(2)}) collective-permute-start(bf16[80,1024]{1,0:T(8,128)(2,1)S(1)} %add_convert_fusion), channel_id=1, source_target_pairs={{0,24},{2,26},{4,28},{6,30},{8,16},{10,18},{12,20},{14,22},{16,8},... | collective-permute-start | bytes 491528 | tf_op jit(solution)/shard_map/ppermute | solution.py:32
  212.6 17.3 %collective-permute-start.31 = (bf16[80,1024]{1,0:T(8,128)(2,1)S(1)}, bf16[80,1024]{1,0:T(8,128)(2,1)S(1)}, u32[]{:S(2)}, u32[]{:S(2)}) collective-permute-start(bf16[80,1024]{1,0:T(8,128)(2,1)S(1)} %add_convert_fusion), channel_id=1, source_target_pairs={{0,16},{2,18},{4,20},{6,22},{8,24},{10,26},{12,28},{14,30},{16,0},... | collective-permute-start | bytes 491528 | tf_op jit(solution)/shard_map/ppermute | solution.py:32
  230.1 26.1 %copy-start.2 = (bf16[256,512]{1,0:T(8,128)(2,1)S(1)}, bf16[256,512]{1,0:T(8,128)(2,1)}, u32[]{:S(2)}) copy-start(bf16[256,512]{1,0:T(8,128)(2,1)} %own_ref.1) | copy-start | bytes 786436
  230.1 26.1 %copy-start.4 = (bf16[256,512]{1,0:T(8,128)(2,1)S(1)}, bf16[256,512]{1,0:T(8,128)(2,1)}, u32[]{:S(2)}) copy-start(bf16[256,512]{1,0:T(8,128)(2,1)} %param.25) | copy-start | bytes 786436
  231.0 18.7 %collective-permute-start.33 = (bf16[320,1024]{1,0:T(8,128)(2,1)}, bf16[320,1024]{1,0:T(8,128)(2,1)}, u32[]{:S(2)}, u32[]{:S(2)}) collective-permute-start(bf16[320,1024]{1,0:T(8,128)(2,1)} %pad_maximum_fusion.inner_ref), channel_id=1, source_target_pairs={{0,4},{2,6},{4,0},{6,2},{8,12},{10,14},{12,8},{14,10},{16,20},{18,... | collective-permute-start | bytes 1966088 | tf_op jit(solution)/shard_map/ppermute | solution.py:32
  231.9 24.4 %collective-permute-start.16 = (f32[256,512]{1,0:T(8,128)S(1)}, f32[256,512]{1,0:T(8,128)S(1)}, u32[]{:S(2)}, u32[]{:S(2)}) collective-permute-start(f32[256,512]{1,0:T(8,128)S(1)} %slice_select_fusion.1), channel_id=1, source_target_pairs={{0,1},{1,0},{2,3},{3,2},{4,5},{5,4},{6,7},{7,6},{8,9},{9,8},{10,11... | collective-permute-start | bytes 1572872 | tf_op jit(solution)/shard_map/ppermute | solution.py:32
  233.3 22.9 %collective-permute-start.19 = (f32[256,512]{1,0:T(8,128)S(1)}, f32[256,512]{1,0:T(8,128)S(1)}, u32[]{:S(2)}, u32[]{:S(2)}) collective-permute-start(f32[256,512]{1,0:T(8,128)S(1)} %slice_select_fusion), channel_id=1, source_target_pairs={{0,1},{1,0},{2,3},{3,2},{4,5},{5,4},{6,7},{7,6},{8,9},{9,8},{10,11... | collective-permute-start | bytes 1572872 | tf_op jit(solution)/shard_map/ppermute | solution.py:32
  234.1 22.1 %collective-permute-start.20 = (f32[256,1]{0,1:T(1,128)S(1)}, f32[256,1]{0,1:T(1,128)S(1)}, u32[]{:S(2)}, u32[]{:S(2)}) collective-permute-start(f32[256,1]{0,1:T(1,128)S(1)} %bitcast.100), channel_id=1, source_target_pairs={{0,1},{1,0},{2,3},{3,2},{4,5},{5,4},{6,7},{7,6},{8,9},{9,8},{10,11... | collective-permute-start | bytes 3080 | tf_op jit(solution)/shard_map/ppermute | solution.py:32
  235.4 88.3 %collective-permute-start.35 = (bf16[320,1024]{1,0:T(8,128)(2,1)}, bf16[320,1024]{1,0:T(8,128)(2,1)}, u32[]{:S(2)}, u32[]{:S(2)}) collective-permute-start(bf16[320,1024]{1,0:T(8,128)(2,1)} %pad_maximum_fusion.inner_ref), channel_id=1, source_target_pairs={{0,2},{2,0},{4,6},{6,4},{8,10},{10,8},{12,14},{14,12},{16,18},{18,... | collective-permute-start | bytes 1966088 | tf_op jit(solution)/shard_map/ppermute | solution.py:32
  249.7 82.1 %collective-permute-start.34 = (bf16[320,1024]{1,0:T(8,128)(2,1)}, bf16[320,1024]{1,0:T(8,128)(2,1)}, u32[]{:S(2)}, u32[]{:S(2)}) collective-permute-start(bf16[320,1024]{1,0:T(8,128)(2,1)} %collective-permute-done.33.inner_ref), channel_id=1, source_target_pairs={{0,2},{2,0},{4,6},{6,4},{8,10},{10,8},{12,14},{14,12},{16,18},{18,... | collective-permute-start | bytes 1966088 | tf_op jit(solution)/shard_map/ppermute | solution.py:32
  323.7 2.9 slice-start
  323.7 2.9 slice-start.1
  335.3 7.8 %collective-permute-start.36 = (f32[1,1024]{1,0:T(1,128)S(1)}, f32[1,1024]{1,0:T(1,128)S(1)}, u32[]{:S(2)}, u32[]{:S(2)}) collective-permute-start(f32[1,1024]{1,0:T(1,128)S(1)} %slice.243), channel_id=1, source_target_pairs={{0,1},{1,0},{2,3},{3,2},{4,5},{5,4},{6,7},{7,6},{8,9},{9,8},{10,11... | collective-permute-start | bytes 12296 | tf_op jit(solution)/shard_map/ppermute | solution.py:32
Sparse Core Ops, SparseCore 0:
  101.1 60.6 reduce-scatter.1
  166.4 111.7 all-reduce.2
  280.3 40.6 all-gather.1

commit v6 on v5

--- a/solution.py
+++ b/solution.py
@@ -268,9 +268,9 @@
 
 
 def scan_ends(
-    part, selected, other, step_weight, step_bias, act, projected, gated_grad, masks, decay_log
+    selected, other, step_weight, step_bias, act, projected, gated_grad, masks, decay_log
 ):
-    rows, width = act.shape[0], scan_width
+    rows, width = act.shape
     count = decay_log.shape[0]
     columns = selected.shape[0]
     rank = step_weight.shape[0]
@@ -281,13 +281,13 @@
         [
             whole_spec(columns, rows),
             whole_spec(columns, rows),
-            column_spec(rank, part),
-            column_spec(1, part),
-            column_spec(rows, part),
-            part_spec(1, rows, part),
-            column_spec(rows, part),
+            column_spec(rank),
+            column_spec(1),
+            column_spec(rows),
+            part_spec(1, rows),
+            column_spec(rows),
             whole_spec(rows, masks.shape[1]),
-            column_spec(count, part),
+            column_spec(count),
         ],
         [column_spec(rows), column_spec(rows), column_spec(2 * count + 8)],
         [
@@ -296,7 +296,7 @@
             jax.ShapeDtypeStruct((2 * count + 8, width), f32),
         ],
         [pltpu.VMEM((2 * count, rows), f32)] + [pltpu.VMEM((rows, scan_width), f32)] * 3,
-        5_000_000_000,
+        10_000_000_000,
         selected,
         other,
         step_weight,
@@ -344,7 +344,98 @@
     return total[:1, :]
 
 
-def scan_kernel(
+def at_token(t, count):
+    return pl.ds(pl.multiple_of(t * count, count), count)
+
+
+def forward_kernel(
+    selected_ref,
+    other_ref,
+    step_ref,
+    act_ref,
+    gate_ref,
+    gated_grad_ref,
+    mask_ref,
+    decay_log_ref,
+    entry_ref,
+    skip_ref,
+    pair_ref,
+    coef,
+    held_step,
+    drive,
+    scanned,
+    halves,
+):
+    rows = step_ref.shape[0]
+    count = decay_log_ref.shape[0]
+    rank = selected_ref.shape[0] - 2 * count
+    decay2 = -jnp.exp(decay_log_ref[...]) * log2e
+    coef[...] = selected_ref[rank:, :] + other_ref[rank:, :]
+    act = act_ref[...].astype(f32)
+    held_step[...] = jnp.where(mask_ref[:, 1:2] > 0.0, step_ref[...], reset_step)
+    drive[...] = step_ref[...] * act
+
+    def forward(block, state):
+        columns = coef_columns(coef, block)
+        for i in range(body_rows):
+            row = pl.ds(block * body_rows + i, 1)
+            factor = jnp.exp2(held_step[row, :] * decay2)
+            state = factor * state + columns[:count, i : i + 1] * drive[row, :]
+            keep_halves(halves, i, columns[count:, i : i + 1] * state)
+        put_state_sums(halves, scanned, block)
+        return state
+
+    lax.fori_loop(0, rows // body_rows, forward, entry_ref[...])
+    gate = gate_ref[...].astype(f32)
+    logistic = jax.nn.sigmoid(gate)
+    total = scanned[...] + skip_ref[...] * act
+    pair_ref[0] = (total * (gate * logistic)).astype(bf16)
+    slope = logistic * (1.0 + gate * (1.0 - logistic))
+    pair_ref[1] = (gated_grad_ref[...] * total * slope).astype(bf16)
+
+
+def scan_forward(
+    selected, other, step, act, projected, gated_grad, masks, decay_log, entry, skip_gain
+):
+    rows, width = step.shape
+    count = decay_log.shape[0]
+    columns = selected.shape[0]
+    return call(
+        forward_kernel,
+        "scan_forward",
+        width,
+        [
+            whole_spec(columns, rows),
+            whole_spec(columns, rows),
+            column_spec(rows),
+            column_spec(rows),
+            part_spec(1, rows),
+            column_spec(rows),
+            whole_spec(rows, masks.shape[1]),
+            column_spec(count),
+            column_spec(count),
+            column_spec(1),
+        ],
+        pl.BlockSpec((2, rows, scan_width), lambda j: (0, 0, j)),
+        jax.ShapeDtypeStruct((2, rows, width), bf16),
+        [pltpu.VMEM((2 * count, rows), f32)]
+        + [pltpu.VMEM((rows, scan_width), f32)] * 3
+        + [pltpu.VMEM((8 * body_rows * (scan_width // lanes), lanes), f32)],
+        10_000_000_000,
+        selected,
+        other,
+        step,
+        act,
+        projected,
+        gated_grad,
+        masks,
+        decay_log,
+        entry,
+        skip_gain,
+    )
+
+
+def backward_kernel(
     selected_ref,
     other_ref,
     step_pre_ref,
@@ -358,12 +449,10 @@
     tail_ref,
     skip_ref,
     step_weight_ref,
-    before_ref,
     *rest,
     waits,
 ):
     (
-        pair_ref,
         act_grad_ref,
         select_grad_ref,
         small_ref,
@@ -371,8 +460,8 @@
         held_step,
         drive,
         scan_grad,
-        scanned,
         weighted,
+        held_sum,
         states,
         factors,
         halves,
@@ -393,10 +482,17 @@
     act = act_ref[...].astype(f32)
     held_step[...] = jnp.where(mask_ref[:, 1:2] > 0.0, step, reset_step)
     drive[...] = step * act
+    gate = gate_ref[...].astype(f32)
+    grads = gated_grad_ref[...] * (gate * jax.nn.sigmoid(gate))
+    scan_grad[...] = grads
+    small_ref[rank + count : rank + count + 1, :] = jnp.sum(grads * act, axis=0, keepdims=True)
     states[:count, :] = entry_ref[...]
 
-    def at_token(t):
-        return pl.ds(pl.multiple_of(t * count, count), count)
+    @pl.when(pl.program_id(0) == 0)
+    def _():
+        in_sum[...] = jnp.zeros(in_sum.shape, f32)
+        read_sum[...] = jnp.zeros(read_sum.shape, f32)
+        select_grad_ref[...] = jnp.zeros(select_grad_ref.shape, f32)
 
     def forward(block, state):
         columns = coef_columns(coef, block)
@@ -405,25 +501,11 @@
             row = pl.ds(t, 1)
             factor = jnp.exp2(held_step[row, :] * decay2)
             state = factor * state + columns[:count, i : i + 1] * drive[row, :]
-            factors[at_token(t), :] = factor
-            states[at_token(t + 1), :] = state
-            keep_halves(halves, i, columns[count:, i : i + 1] * state)
-        put_state_sums(halves, scanned, block)
+            factors[at_token(t, count), :] = factor
+            states[at_token(t + 1, count), :] = state
         return state
 
     lax.fori_loop(0, blocks, forward, entry_ref[...])
-
-    gate = gate_ref[...].astype(f32)
-    logistic = jax.nn.sigmoid(gate)
-    gate_act = gate * logistic
-    gated_grad = gated_grad_ref[...]
-    grads = gated_grad * gate_act
-    scan_grad[...] = grads
-    total = scanned[...] + skip_ref[...] * act
-    pair_ref[0] = (total * gate_act).astype(bf16)
-    slope = logistic * (1.0 + gate * (1.0 - logistic))
-    pair_ref[1] = (gated_grad * total * slope).astype(bf16)
-    small_ref[rank + count : rank + count + 1, :] = jnp.sum(grads * act, axis=0, keepdims=True)
 
     def backward(k, carried):
         adjoint, decay_grad = carried
@@ -432,24 +514,25 @@
         for i in range(body_rows - 1, -1, -1):
             t = block * body_rows + i
             row = pl.ds(t, 1)
+            here = at_token(t, count)
             grad = scan_grad[row, :]
             summed = columns[count:, i : i + 1] * grad + adjoint
-            read_sum[at_token(t), :] = tree_sum(lane_tiles(grad * states[at_token(t + 1), :]))
-            in_sum[at_token(t), :] = tree_sum(lane_tiles(summed * drive[row, :]))
+            read_sum[here, :] += tree_sum(lane_tiles(grad * states[at_token(t + 1, count), :]))
+            in_sum[here, :] += tree_sum(lane_tiles(summed * drive[row, :]))
             keep_halves(halves, i, summed * columns[:count, i : i + 1])
-            adjoint = factors[at_token(t), :] * summed
-            held = adjoint * states[at_token(t), :]
+            adjoint = factors[here, :] * summed
+            held = adjoint * states[here, :]
             decay_grad = decay_grad + held * step_ref[row, :]
             keep_halves(more_halves, i, held * decay)
         put_state_sums(halves, weighted, block)
-        put_state_sums(more_halves, scanned, block)
+        put_state_sums(more_halves, held_sum, block)
         return adjoint, decay_grad
 
     ignored, decay_grad = lax.fori_loop(
         0, blocks, backward, (tail_ref[...], jnp.zeros(decay.shape, f32))
     )
     act_grad_ref[...] = step * weighted[...] + skip_ref[...] * scan_grad[...]
-    step_grad = act * weighted[...] + scanned[...]
+    step_grad = act * weighted[...] + held_sum[...]
     pre_grad = (step_grad * jax.nn.sigmoid(step_pre_ref[...])).astype(bf16)
     small_ref[:rank, :] = jnp.dot(step_low, pre_grad, preferred_element_type=f32)
     small_ref[rank : rank + count, :] = decay_grad * decay
@@ -457,19 +540,19 @@
     small_ref[rank + count + 1 : rank + count + 2, :] = bias_grad
     spare = small_ref.shape[0] - (rank + count + 2)
     small_ref[rank + count + 2 :, :] = jnp.zeros((spare, small_ref.shape[1]), f32)
-    before = before_ref[...]
-    select_grad_ref[:rank, :] = before[:rank] + lax.dot_general(
+    select_grad_ref[:rank, :] += lax.dot_general(
         step_weight_ref[...], pre_grad, contract_last, preferred_element_type=f32
     )
-    for n in range(count):
-        at = pl.ds(n, rows, stride=count)
-        low, high = rank + n, rank + count + n
-        select_grad_ref[low : low + 1, :] = before[low : low + 1] + lane_sums(in_sum[at, :])
-        select_grad_ref[high : high + 1, :] = before[high : high + 1] + lane_sums(read_sum[at, :])
-
-
-def scan_full(
-    part,
+
+    @pl.when(pl.program_id(0) == pl.num_programs(0) - 1)
+    def _():
+        for n in range(count):
+            at = pl.ds(n, rows, stride=count)
+            select_grad_ref[rank + n : rank + n + 1, :] = lane_sums(in_sum[at, :])
+            select_grad_ref[rank + count + n : rank + count + n + 1, :] = lane_sums(read_sum[at, :])
+
+
+def scan_backward(
     selected,
     other,
     step_pre,
@@ -483,7 +566,6 @@
     tail,
     skip_gain,
     step_weight,
-    before,
     waits,
 ):
     rows, width = step.shape
@@ -493,34 +575,27 @@
     half_rows = 8 * body_rows * (scan_width // lanes)
     small = rank + count + 16
     return call(
-        functools.partial(scan_kernel, waits=len(waits)),
-        "scan_full",
+        functools.partial(backward_kernel, waits=len(waits)),
+        "scan_backward",
         width,
         [
             whole_spec(columns, rows),
             whole_spec(columns, rows),
             column_spec(rows),
             column_spec(rows),
-            column_spec(rows, part),
-            part_spec(1, rows, part),
-            column_spec(rows, part),
+            column_spec(rows),
+            part_spec(1, rows),
+            column_spec(rows),
             whole_spec(rows, masks.shape[1]),
-            column_spec(count, part),
             column_spec(count),
             column_spec(count),
-            column_spec(1, part),
-            column_spec(rank, part),
-            whole_spec(columns, rows),
+            column_spec(count),
+            column_spec(1),
+            column_spec(rank),
         ]
         + [pl.BlockSpec(memory_space=pl.ANY)] * len(waits),
+        [column_spec(rows), whole_spec(columns, rows), column_spec(small)],
         [
-            pl.BlockSpec((2, rows, scan_width), lambda j: (0, 0, j)),
-            column_spec(rows),
-            whole_spec(columns, rows),
-            column_spec(small),
-        ],
-        [
-            jax.ShapeDtypeStruct((2, rows, width), bf16),
             jax.ShapeDtypeStruct((rows, width), f32),
             jax.ShapeDtypeStruct((columns, rows), f32),
             jax.ShapeDtypeStruct((small, width), f32),
@@ -535,7 +610,7 @@
             pltpu.VMEM((rows * count, lanes), f32),
             pltpu.VMEM((rows * count, lanes), f32),
         ],
-        13_000_000_000,
+        22_000_000_000,
         selected,
         other,
         step_pre,
@@ -549,7 +624,6 @@
         tail,
         skip_gain,
         step_weight,
-        before,
         *waits,
     )
 
@@ -608,9 +682,9 @@
 
 
 def convolve_grad(
-    part, select_grad, other, select_weight, act_grad, convolved, act, projected, conv_weight, masks
+    select_grad, other, select_weight, act_grad, convolved, act, projected, conv_weight, masks
 ):
-    rows, width = act_grad.shape
+    rows, width = act.shape
     extended = rows + halo
     columns = select_weight.shape[0]
     taps = conv_weight.shape[0]
@@ -622,12 +696,12 @@
         [
             whole_spec(columns, rows),
             whole_spec(columns, rows),
-            column_spec(columns, part),
+            column_spec(columns),
             column_spec(rows),
-            column_spec(rows, part),
-            column_spec(rows, part),
-            part_spec(0, extended, part),
-            column_spec(taps, part),
+            column_spec(rows),
+            column_spec(rows),
+            part_spec(0, extended),
+            column_spec(taps),
             whole_spec(rows, masks.shape[1]),
         ],
         [column_spec(rows), column_spec(16), column_spec(small)],
@@ -637,7 +711,7 @@
             jax.ShapeDtypeStruct((small, width), f32),
         ],
         [pltpu.VMEM((extended, scan_width), f32), pltpu.VMEM((rows + 16, scan_width), f32)],
-        3_000_000_000,
+        5_000_000_000,
         select_grad,
         other,
         select_weight,
@@ -748,12 +822,10 @@
     )(place, own, near, far, last, normed, small)
 
 
-def join_kernel(place_ref, first_ref, second_ref, inner_ref, *rest):
+def join_kernel(place_ref, gate_ref, inner_ref, *rest):
     out_ref, small_ref = rest[-2:]
-    half = out_ref.shape[2] // 2
     rows, spare = out_ref.shape[0] // 2, small_ref.shape[0] // 2
-    out_ref[:, 1, :half] = first_ref[...].astype(f32)
-    out_ref[:, 1, half:] = second_ref[...].astype(f32)
+    out_ref[:, 1, :] = gate_ref[...].astype(f32)
     for n in range(2):
         at = n * (rows + spare)
         block = inner_ref[at : at + rows + spare, :].astype(f32)
@@ -761,15 +833,10 @@
         small_ref[n * spare : (n + 1) * spare, :] = block[rows:]
 
 
-def joined(place, flip, first, second, inner, before, waits):
-    depth = first.shape[0]
-    quarter, width = depth // 4, 2 * scan_width
+def joined(place, flip, gate, inner, before, waits):
+    depth, width = gate.shape
+    quarter = depth // 4
     small = inner.shape[0] - quarter
-
-    def source(j, place):
-        number = place[0] ^ flip
-        return 4 + 2 * lax.rem(number, 2) + j, number // 2
-
     untouched = [*before, *waits]
     return pl.pallas_call(
         join_kernel,
@@ -777,8 +844,7 @@
             num_scalar_prefetch=1,
             grid=(2,),
             in_specs=[
-                pl.BlockSpec((quarter // 2, scan_width), source),
-                pl.BlockSpec((quarter // 2, scan_width), source),
+                pl.BlockSpec((quarter // 2, width), lambda j, place: (2 * (place[0] ^ flip) + j, 0)),
                 pl.BlockSpec((inner.shape[0] // 2, width), lambda j, place: (j, 0)),
             ]
             + [pl.BlockSpec(memory_space=pl.ANY)] * len(untouched),
@@ -793,10 +859,24 @@
             jax.ShapeDtypeStruct((depth, 2, width), f32),
             jax.ShapeDtypeStruct((4 * small, width), f32),
         ],
-        input_output_aliases={4 + k: k for k in range(len(before))},
+        input_output_aliases={3 + k: k for k in range(len(before))},
         compiler_params=pltpu.CompilerParams(vmem_limit_bytes=vmem_bytes),
         name="joined",
-    )(place, first, second, inner, *untouched)
+    )(place, gate, inner, *untouched)
+
+
+def parts_kernel(small_ref, *out_refs, starts):
+    for ref, start in zip(out_refs, starts):
+        ref[...] = small_ref[start : start + ref.shape[0], :]
+
+
+def small_parts(small, sizes):
+    width = small.shape[1]
+    return pl.pallas_call(
+        functools.partial(parts_kernel, starts=[start for start, _ in sizes]),
+        out_shape=[jax.ShapeDtypeStruct((rows, width), f32) for _, rows in sizes],
+        name="small_parts",
+    )(small)
 
 
 def carried(ends, decay):
@@ -891,66 +971,55 @@
     gated_grad = lax.dot_general(
         cot_whole, out_weight, contract_last, preferred_element_type=f32
     )
-    parts = range(out_weight.shape[0] // scan_width)
-    decay = -jnp.exp(decay_log)
-    started = []
-    for part in parts:
-        step_pre, step, ends = scan_ends(
-            part,
-            selected,
-            other_selected,
-            step_weight,
-            step_bias[None],
-            act,
-            projected,
-            gated_grad,
-            masks,
-            decay_log,
-        )
-        here = decay[:, part * scan_width : (part + 1) * scan_width]
-        started.append((step_pre, step, carried(ends, here)))
+    step_pre, step, ends = scan_ends(
+        selected,
+        other_selected,
+        step_weight,
+        step_bias[None],
+        act,
+        projected,
+        gated_grad,
+        masks,
+        decay_log,
+    )
+    entry, tail = carried(ends, -jnp.exp(decay_log))
+    pair = scan_forward(
+        selected,
+        other_selected,
+        step,
+        act,
+        projected,
+        gated_grad,
+        masks,
+        decay_log,
+        entry,
+        skip_gain[None],
+    )
+    gated, gate_grad = pair[0], pair[1]
     normed = normed_ext[:rows]
     normed_four = quarter_of_four(normed)
-    select_grad = jnp.zeros(selected.shape, f32)
-    waits = [[started[-1][2][0]], [normed_four]]
-    done, sums = [], []
-    for part in parts:
-        step_pre, step, (entry, tail) = started[part]
-        pair, act_grad, select_grad, small = scan_full(
-            part,
-            selected,
-            other_selected,
-            step_pre,
-            step,
-            act,
-            projected,
-            gated_grad,
-            masks,
-            decay_log,
-            entry,
-            tail,
-            skip_gain[None],
-            step_weight,
-            select_grad,
-            waits[part],
-        )
-        done.append((pair, act_grad, small))
-        out_rows = lax.dot_general(pair[0], cot_whole, contract_first, preferred_element_type=f32)
-        gate_rows = lax.dot_general(normed, pair[1], contract_first, preferred_element_type=f32)
-        half = gate_rows.shape[0] // 2
-        product = jnp.concatenate(
-            [out_rows, jnp.concatenate([gate_rows[:half], gate_rows[half:]], axis=1)]
-        ).astype(bf16)
-        waits[-1].append(product)
-        if part == 0:
-            share = lax.psum_scatter(product, "wide", scatter_dimension=0, tiled=True)
-            sums.append(lax.all_gather(share, "wide", axis=0, tiled=True))
-        else:
-            sums.append(lax.psum(product, "wide"))
+    products = (
+        lax.dot_general(gated, cot_whole, contract_first, preferred_element_type=f32).astype(bf16),
+        lax.dot_general(normed, gate_grad, contract_first, preferred_element_type=f32).astype(bf16),
+    )
+    out_sum, gate_sum = lax.psum(products, "wide")
+    act_grad, select_grad, scan_small = scan_backward(
+        selected,
+        other_selected,
+        step_pre,
+        step,
+        act,
+        projected,
+        gated_grad,
+        masks,
+        decay_log,
+        entry,
+        tail,
+        skip_gain[None],
+        step_weight,
+        [normed_four, *products],
+    )
     other_select_grad = swapped(select_grad, "narrow", 1)
-    scan_small = jnp.concatenate([small for _, _, small in done], axis=1)
-    gated = jnp.concatenate([pair[0] for pair, _, _ in done], axis=1)
-    gate_grad = jnp.concatenate([pair[1] for pair, _, _ in done], axis=1)
 
     def narrow_halves(array):
         low, high = array[:, :features], array[:, features:]
@@ -958,25 +1027,20 @@
 
     out_part = jnp.dot(gated, out_weight, preferred_element_type=f32)
     out_mine, out_other = narrow_halves(out_part)
-    out_sum = out_mine + swapped(out_other, "narrow", 1)
-    layer_out = (tokens.astype(f32) + out_sum).astype(bf16)
-
-    results = [
-        convolve_grad(
-            part,
-            select_grad,
-            other_select_grad,
-            select_weight,
-            done[part][1],
-            convolved,
-            act,
-            projected,
-            conv_weight,
-            masks,
-        )
-        for part in parts
-    ]
-    inner_main, edges, conv_small = [jnp.concatenate(x, axis=1) for x in zip(*results)]
+    out_total = out_mine + swapped(out_other, "narrow", 1)
+    layer_out = (tokens.astype(f32) + out_total).astype(bf16)
+
+    inner_main, edges, conv_small = convolve_grad(
+        select_grad,
+        other_select_grad,
+        select_weight,
+        act_grad,
+        convolved,
+        act,
+        projected,
+        conv_weight,
+        masks,
+    )
     from_next = passed_along(edges[:8], "wide", -1)
     last_rows = edges[8:] + jnp.where(same_as_last, from_next, 0.0)
     inner_grad = jnp.concatenate([inner_main[: rows - 8], last_rows.astype(bf16)])
@@ -987,9 +1051,10 @@
     gain_part = jnp.sum(normed_part * whole * inverse, axis=0, keepdims=True)
     row_part = jnp.sum(normed_part * norm_gain * whole, axis=1, keepdims=True)
 
+    gain_sum = gain_part + swapped(gain_part, "narrow", 1)
     spare = -(scan_small.shape[0] + conv_small.shape[0] + 1) % 256
     small = jnp.concatenate(
-        [scan_small, conv_small, gain_part, jnp.zeros((spare, gain_part.shape[1]), f32)]
+        [scan_small, conv_small, gain_sum, jnp.zeros((spare, gain_sum.shape[1]), f32)]
     )
     small_piece = scattered(small, (1, 2))
     near = swapped(inner_grad, "wide", 2)
@@ -1021,7 +1086,7 @@
     ) * (row_sum / (2 * features))
     tokens_grad = (whole_grad + cotangent.astype(f32)).astype(bf16)
 
-    out_weight_grad = jnp.concatenate([total[:scan_width] for total in sums]).astype(f32)
+    out_weight_grad = out_sum.astype(f32)
     near = swapped(held, "wide", 2)
     quarters = (held, swapped(held, "wide", 1), near, swapped(near, "wide", 1))
     results = []
@@ -1029,29 +1094,48 @@
         results = joined(
             (wide_place & 3)[None],
             flip,
-            *sums,
+            gate_sum,
             quarter,
             results,
-            [layer_out, tokens_grad, out_weight_grad] if flip == 2 else [],
+            [layer_out, tokens_grad] if flip == 1 else [],
         )
     in_weight_grad, small_sum = results
-    scan_sum = small_sum[: scan_small.shape[0]]
-    conv_sum = small_sum[scan_small.shape[0] : scan_small.shape[0] + conv_small.shape[0]]
-    gain_row = scan_small.shape[0] + conv_small.shape[0]
-    gain_sum = small_sum[gain_row : gain_row + 1]
-    norm_gain_grad = (gain_sum + swapped(gain_sum, "narrow", 1))[0]
+    conv_at = scan_small.shape[0]
+    gain_at = conv_at + conv_small.shape[0]
+    (
+        step_weight_grad,
+        decay_log_grad,
+        skip_gain_grad,
+        step_bias_grad,
+        select_weight_grad,
+        conv_weight_grad,
+        conv_bias_grad,
+        norm_gain_grad,
+    ) = small_parts(
+        small_sum,
+        [
+            (0, rank),
+            (rank, count),
+            (rank + count, 1),
+            (rank + count + 1, 1),
+            (conv_at, columns),
+            (conv_at + columns, taps),
+            (conv_at + columns + taps, 1),
+            (gain_at, 1),
+        ],
+    )
     return (
         layer_out,
         tokens_grad,
-        norm_gain_grad,
+        norm_gain_grad[0],
         in_weight_grad,
-        conv_sum[columns : columns + taps],
-        conv_sum[columns + taps],
-        conv_sum[:columns],
-        scan_sum[:rank],
-        scan_sum[rank + count + 1],
-        scan_sum[rank : rank + count],
-        scan_sum[rank + count],
+        conv_weight_grad,
+        conv_bias_grad[0],
+        select_weight_grad,
+        step_weight_grad,
+        step_bias_grad[0],
+        decay_log_grad,
+        skip_gain_grad[0],
         out_weight_grad,
     )
 

time: 353 us -> 331 us (0.938)
  starting transfers between devices: 53 us -> 44.8 us
  local copies, waits for them, and re-layouts: 19.3 us -> 11.6 us
    psum x1, waiting for transfers between devices: 20.8 us -> 70 us  [local(): out_sum, gate_sum = lax.psum(products, 'wide')]
    all_gather x1 -> x0, waiting for transfers between devices: 42.9 us -> none  [local(): sums.append(lax.all_gather(share, 'wide', axis=0, tiled=True))]
    ppermute x30 -> x28, waiting for transfers between devices: 83 us -> 75 us  [swapped(): return lax.ppermute(array, axis, [(i, i ^ bit) for i in range(peers)])]
    slice x11 -> x3, local copies, waits for them, and re-layouts: 7.18 us -> 1.07 us  [the longest x1 1.07 us: local(): inner_main[:rows - 8]]
    ppermute x6 -> x4, starting transfers between devices: 14.4 us -> 8.81 us  [passed_along(): return lax.ppermute(array, axis, pairs)]
    ppermute x30 -> x28, starting transfers between devices: 32.6 us -> 30.3 us  [swapped(): return lax.ppermute(array, axis, [(i, i ^ bit) for i in range(peers)])]
    pallas_call x7 -> x5, Pallas kernels: 54.5 us -> 53.6 us  [call(): pl.pallas_call(kernel, grid=(width // scan_width,), in_specs=in_specs, ou...]
  transfers between devices with their start and end apart: 40 -> 34, of which waited for: 19 -> 18; matrix products, arithmetic and copies ran while one was open for 13% -> 9% of each run, Pallas kernels for 13% -> 4%
where the time goes in v6:
time: 331 us; the launch traced here: 330 us
  waiting for transfers between devices  149 us (45%)
  Pallas kernels  73.4 us (22%)
  starting transfers between devices  44.8 us (14%)
  other arithmetic  20.8 us (6%)
  matrix products  16 us (5%)
  between operations  14.5 us (4%)
  local copies, waits for them, and re-layouts  11.6 us (4%)
    ppermute x28, waiting for transfers between devices, swapped(): return lax.ppermute(array, axis, [(i, i ^ bit) for i in range(peers)])  75 us
    psum x1, waiting for transfers between devices, local(): out_sum, gate_sum = lax.psum(products, 'wide')  70 us
    pallas_call x5, Pallas kernels, call(): pl.pallas_call(kernel, grid=(width // scan_width,), in_specs=in_specs, ou...  53.6 us
    ppermute x28, starting transfers between devices, swapped(): return lax.ppermute(array, axis, [(i, i ^ bit) for i in range(peers)])  30.3 us
    pallas_call x4, Pallas kernels, joined(): pl.pallas_call(join_kernel, grid_spec=pltpu.PrefetchScalarGridSpec(num_sc...  10.6 us
    ppermute x4, starting transfers between devices, passed_along(): return lax.ppermute(array, axis, pairs)  8.81 us
  transfers between devices with their start and end apart: 34, of which 18 were waited for; matrix products, arithmetic and copies ran while one was open for 9% of the time, Pallas kernels for 4%

profile of v6, /device:TPU:0, one launch (start us, length us, event | category | flops | bytes accessed | tf_op | source)
XLA Modules:
  0.0 329.9 jit_solution(6203168375245228021)
XLA Ops:
  7.2 1.5 edge_rows.1
  8.7 2.3 collective-permute-start.1
  11.0 5.6 %collective-permute-start.2 = (bf16[16,512]{1,0:T(8,128)(2,1)}, bf16[16,512]{1,0:T(8,128)(2,1)S(1)}, u32[]{:S(2)}, u32[]{:S(2)}) collective-permute-start(bf16[16,512]{1,0:T(8,128)(2,1)} %edge_rows.1), channel_id=1, source_target_pairs={{0,3},{1,2},{2,5},{3,4},{4,7},{5,6},{6,9},{7,8},{8,11},{9,10},{10,... | collective-permute-start | bytes 49160 | tf_op jit(solution)/shard_map/ppermute | solution.py:50
  17.3 1.5 collective-permute-start.4
  18.8 1.3 fusion.39
  20.1 1.5 compare_convert_fusion
  22.5 3.7 %collective-permute-done.other_ref = bf16[256,512]{1,0:T(8,128)(2,1)S(1)} collective-permute-done((bf16[256,512]{1,0:T(8,128)(2,1)}, bf16[256,512]{1,0:T(8,128)(2,1)S(1)}, u32[]{:S(2)}, u32[]{:S(2)}) %collective-permute-start) | collective-permute-done | bytes 262176 | tf_op jit(solution)/shard_map/ppermute | solution.py:32
  26.9 2.2 normalized.1
  29.1 4.9 %fusion.7.inner_ref.gate_ref = bf16[2,272,1024]{2,1,0:T(8,128)(2,1)} fusion(bf16[1024,2,1024]{2,1,0:T(2,128)(2,1)} %param.15, bf16[272,1024]{1,0:T(8,128)(2,1)} %get-tuple-element.45), kind=kOutput, calls=%fused_computation.7 | convolution fusion | flops 1141407744 | bytes 5865472 | tf_op jit(solution)/shard_map/td,dce->cte/dot_general | solution.py:963
  34.0 3.6 %convolve.1 = (f32[256,1024]{1,0:T(8,128)}, bf16[256,1024]{1,0:T(8,128)(2,1)}, f32[96,256]{1,0:T(8,128)}) custom-call(bf16[2,272,1024]{2,1,0:T(8,128)(2,1)} %fusion.7.inner_ref.gate_ref, f32[4,1024]{1,0:T(4,128)} %conv_weight_ref.3, f32[1,1024]{1,0:T(1,128)} %bitcast.77, bf16[96,1024]{1,0:T(8,128)(2,1)} %select_ref.3, f32[256,8]{1,0:T(8,128)} %copy.39.mask_ref), custom_call_target="tpu_custom_call" | custom-call | flops 4000000000 | bytes 1339392 | tf_op jit(solution)/shard_map/convolve/pallas_call | solution.py:129
  38.9 1.7 fusion.27.gated_grad_ref
  40.6 1.8 collective-permute-done.3.other_ref
  43.1 10.8 %scan_ends.1 = (f32[256,1024]{1,0:T(8,128)}, f32[256,1024]{1,0:T(8,128)}, f32[40,1024]{1,0:T(8,128)}) custom-call(f32[96,256]{1,0:T(8,128)} %get-tuple-element.46.selected_ref, f32[96,256]{1,0:T(8,128)} %copy-done.28, bf16[64,1024]{1,0:T(8,128)(2,1)} %step_weight_ref.3, f32[1,1024]{1,0:T(1,128)} %bitcast.78, bf16[256,1024]{1,0:T(8,128)(2,1)} %get-tuple-element.47.act_ref, ...), custom_call_target="tpu_custom_call" | custom-call | flops 10000000000 | bytes 3092480 | tf_op jit(solution)/shard_map/scan_ends/pallas_call | solution.py:129
  54.0 1.6 collective-permute-done.5
  57.9 1.6 collective-permute-start.6
  60.2 1.7 collective-permute-start.12
  61.8 3.5 %collective-permute-done.6 = f32[40,1024]{1,0:T(8,128)} collective-permute-done((f32[40,1024]{1,0:T(8,128)}, f32[40,1024]{1,0:T(8,128)}, u32[]{:S(2)}, u32[]{:S(2)}) %collective-permute-start.6) | collective-permute-done | bytes 163872 | tf_op jit(solution)/shard_map/ppermute | solution.py:32
  67.0 3.5 %collective-permute-start.7 = (f32[16,1024]{1,0:T(8,128)S(1)}, f32[16,1024]{1,0:T(8,128)S(1)}, u32[]{:S(2)}, u32[]{:S(2)}) collective-permute-start(f32[16,1024]{1,0:T(8,128)S(1)} %get-tuple-element.120), channel_id=1, source_target_pairs={{0,8},{2,10},{4,12},{6,14},{8,16},{10,18},{12,20},{14,22},{16,24},... | collective-permute-start | bytes 196616 | tf_op jit(solution)/shard_map/ppermute | solution.py:27
  70.5 1.5 collective-permute-start.9
  72.9 3.8 %collective-permute-done.9 = f32[16,1024]{1,0:T(8,128)S(1)} collective-permute-done((f32[16,1024]{1,0:T(8,128)S(1)}, f32[16,1024]{1,0:T(8,128)S(1)}, u32[]{:S(2)}, u32[]{:S(2)}) %collective-permute-start.9) | collective-permute-done | bytes 65568 | tf_op jit(solution)/shard_map/ppermute | solution.py:27
  76.7 1.6 multiply_add_fusion
  78.3 10.4 %scan_forward.1 = bf16[2,256,1024]{2,1,0:T(8,128)(2,1)} custom-call(f32[96,256]{1,0:T(8,128)} %get-tuple-element.46.selected_ref, f32[96,256]{1,0:T(8,128)} %copy-done.28, f32[256,1024]{1,0:T(8,128)} %get-tuple-element.48.step_ref, bf16[256,1024]{1,0:T(8,128)(2,1)} %get-tuple-element.47.act_ref, bf16[2,272,1024]{2,1,0:T(8,128)(2,1)} %fusion.7.inner_ref.gate_ref, ...), custom_call_target="tpu_custom_call" | custom-call | flops 10000000000 | bytes 4075520 | tf_op jit(solution)/shard_map/scan_forward/pallas_call | solution.py:129
  88.7 3.2 convolution_convert_fusion.1.rest_1_
  91.9 2.1 convolution_convert_fusion.rest_2_
  94.0 24.1 %scan_backward.1 = (f32[256,1024]{1,0:T(8,128)}, f32[96,256]{1,0:T(8,128)}, f32[96,1024]{1,0:T(8,128)}) custom-call(f32[96,256]{1,0:T(8,128)} %get-tuple-element.46.selected_ref, f32[96,256]{1,0:T(8,128)} %copy-done.28, f32[256,1024]{1,0:T(8,128)} %get-tuple-element.51.step_pre_ref, f32[256,1024]{1,0:T(8,128)} %get-tuple-element.48.step_ref, ...), custom_call_target="tpu_custom_call" | custom-call | flops 22000001024 | bytes 10039296 | tf_op jit(solution)/shard_map/scan_backward/pallas_call | solution.py:129
  119.4 3.6 %collective-permute-done.13.other_ref = f32[96,256]{1,0:T(8,128)S(1)} collective-permute-done((f32[96,256]{1,0:T(8,128)}, f32[96,256]{1,0:T(8,128)S(1)}, u32[]{:S(2)}, u32[]{:S(2)}) %collective-permute-start.13) | collective-permute-done | bytes 98336 | tf_op jit(solution)/shard_map/ppermute | solution.py:32
  123.7 4.8 %convolve_grad.1 = (bf16[256,1024]{1,0:T(8,128)(2,1)}, f32[16,1024]{1,0:T(8,128)}, f32[112,1024]{1,0:T(8,128)}) custom-call(f32[96,256]{1,0:T(8,128)} %get-tuple-element.52.select_grad_ref, f32[96,256]{1,0:T(8,128)} %copy-done.29, bf16[96,1024]{1,0:T(8,128)(2,1)} %select_ref.3, f32[256,1024]{1,0:T(8,128)} %get-tuple-element.53.act_grad_ref, ...), custom_call_target="tpu_custom_call" | custom-call | flops 5000000000 | bytes 4153344 | tf_op jit(solution)/shard_map/convolve_grad/pallas_call | solution.py:129
  129.4 1.5 collective-permute-start.14
  131.6 1.1 slice.114
  132.8 0.9 pad_maximum_fusion.3
  133.7 2.2 collective-permute-start.17
  135.9 3.4 %fusion.15 = (f32[1024]{0:T(1024)S(1)}, f32[256]{0:T(256)}, f32[256,1024]{1,0:T(8,128)}) fusion(f32[256]{0:T(256)S(1)} %get-tuple-element.80, bf16[272,1024]{1,0:T(8,128)(2,1)S(1)} %copy-done.27, f32[1024]{0:T(1024)S(1)} %copy-done.18, bf16[1024,2,1024]{2,1,0:T(2,128)(2,1)S(1)} %copy-done.26, bf16[1,256,1024]{2,1,0:T(8,128)(2,1)S(1)} %slice-done, ...), kind=kOutput, calls=%fused_computation.13 | convolution fusion | flops 1076099840 | bytes 6825984 | tf_op jit(solution)/shard_map/cte,dce->td/dot_general | solution.py:1047
  140.4 2.4 collective-permute-done.20
  142.9 5.5 %collective-permute-done.17.near_ref = bf16[256,1024]{1,0:T(8,128)(2,1)} collective-permute-done((bf16[256,1024]{1,0:T(8,128)(2,1)}, bf16[256,1024]{1,0:T(8,128)(2,1)}, u32[]{:S(2)}, u32[]{:S(2)}) %collective-permute-start.17) | collective-permute-done | bytes 524320 | tf_op jit(solution)/shard_map/ppermute | solution.py:32
  148.8 1.2 maximum_maximum_fusion
  150.0 1.0 copy-done.3
  151.8 2.5 collective-permute-start.22
  154.2 4.5 %collective-permute-done.22 = bf16[64,1024]{1,0:T(8,128)(2,1)S(1)} collective-permute-done((bf16[64,1024]{1,0:T(8,128)(2,1)}, bf16[64,1024]{1,0:T(8,128)(2,1)S(1)}, u32[]{:S(2)}, u32[]{:S(2)}) %collective-permute-start.22) | collective-permute-done | bytes 131104 | tf_op jit(solution)/shard_map/ppermute | solution.py:32
  158.7 1.8 collective-permute-done.23
  160.5 1.7 convert_add_fusion.1.small_ref
  162.2 3.4 %inner_quarter.1 = (f32[80,1024]{1,0:T(8,128)}, bf16[3,80,1024]{2,1,0:T(8,128)(2,1)}) custom-call(s32[1]{0:T(128)} %bitcast.31.place_ref, bf16[256,1024]{1,0:T(8,128)(2,1)} %get-tuple-element.96.own_ref, bf16[256,1024]{1,0:T(8,128)(2,1)} %collective-permute-done.17.near_ref, bf16[256,1024]{1,0:T(8,128)(2,1)} %collective-permute-done.18.far_ref, ...), custom_call_target="tpu_custom_call" | custom-call | flops 2000000000 | bytes 4000000 | tf_op jit(solution)/shard_map/inner_quarter/pallas_call | solution.py:808
  165.6 1.1 slice_bitcast_fusion.5
  166.7 1.5 collective-permute-start.24
  168.8 2.4 collective-permute-start.26
  171.2 5.0 %collective-permute-done.24 = bf16[80,1024]{1,0:T(8,128)(2,1)S(1)} collective-permute-done((bf16[80,1024]{1,0:T(8,128)(2,1)S(1)}, bf16[80,1024]{1,0:T(8,128)(2,1)S(1)}, u32[]{:S(2)}, u32[]{:S(2)}) %collective-permute-start.24) | collective-permute-done | bytes 163872 | tf_op jit(solution)/shard_map/ppermute | solution.py:32
  176.2 7.0 %collective-permute-done.25 = bf16[80,1024]{1,0:T(8,128)(2,1)S(1)} collective-permute-done((bf16[80,1024]{1,0:T(8,128)(2,1)S(1)}, bf16[80,1024]{1,0:T(8,128)(2,1)S(1)}, u32[]{:S(2)}, u32[]{:S(2)}) %collective-permute-start.25) | collective-permute-done | bytes 163872 | tf_op jit(solution)/shard_map/ppermute | solution.py:32
  183.2 1.1 add_convert_fusion
  184.3 3.5 %collective-permute-start.29 = (bf16[80,1024]{1,0:T(8,128)(2,1)S(1)}, bf16[80,1024]{1,0:T(8,128)(2,1)S(1)}, u32[]{:S(2)}, u32[]{:S(2)}) collective-permute-start(bf16[80,1024]{1,0:T(8,128)(2,1)S(1)} %add_convert_fusion), channel_id=1, source_target_pairs={{0,8},{2,10},{4,12},{6,14},{8,0},{10,2},{12,4},{14,6},{16,24},{18,... | collective-permute-start | bytes 491528 | tf_op jit(solution)/shard_map/ppermute | solution.py:32
  187.8 2.2 collective-permute-start.27
  190.0 3.4 %collective-permute-done.29 = bf16[80,1024]{1,0:T(8,128)(2,1)S(1)} collective-permute-done((bf16[80,1024]{1,0:T(8,128)(2,1)S(1)}, bf16[80,1024]{1,0:T(8,128)(2,1)S(1)}, u32[]{:S(2)}, u32[]{:S(2)}) %collective-permute-start.29) | collective-permute-done | bytes 163872 | tf_op jit(solution)/shard_map/ppermute | solution.py:32
  193.5 8.3 %collective-permute-done.27 = bf16[80,1024]{1,0:T(8,128)(2,1)S(1)} collective-permute-done((bf16[80,1024]{1,0:T(8,128)(2,1)S(1)}, bf16[80,1024]{1,0:T(8,128)(2,1)S(1)}, u32[]{:S(2)}, u32[]{:S(2)}) %collective-permute-start.27) | collective-permute-done | bytes 163872 | tf_op jit(solution)/shard_map/ppermute | solution.py:32
  201.7 5.1 %collective-permute-done.28 = bf16[80,1024]{1,0:T(8,128)(2,1)S(1)} collective-permute-done((bf16[80,1024]{1,0:T(8,128)(2,1)S(1)}, bf16[80,1024]{1,0:T(8,128)(2,1)S(1)}, u32[]{:S(2)}, u32[]{:S(2)}) %collective-permute-start.28) | collective-permute-done | bytes 163872 | tf_op jit(solution)/shard_map/ppermute | solution.py:32
  207.9 4.1 %collective-permute-start.30 = (bf16[320,1024]{1,0:T(8,128)(2,1)}, bf16[320,1024]{1,0:T(8,128)(2,1)}, u32[]{:S(2)}, u32[]{:S(2)}) collective-permute-start(bf16[320,1024]{1,0:T(8,128)(2,1)} %pad_maximum_fusion.inner_ref), channel_id=1, source_target_pairs={{0,4},{2,6},{4,0},{6,2},{8,12},{10,14},{12,8},{14,10},{16,20},{18,... | collective-permute-start | bytes 1966088 | tf_op jit(solution)/shard_map/ppermute | solution.py:32
  213.5 1.6 collective-permute-start.15
  215.6 11.1 %collective-permute-done.30.inner_ref = bf16[320,1024]{1,0:T(8,128)(2,1)} collective-permute-done((bf16[320,1024]{1,0:T(8,128)(2,1)}, bf16[320,1024]{1,0:T(8,128)(2,1)}, u32[]{:S(2)}, u32[]{:S(2)}) %collective-permute-start.30) | collective-permute-done | bytes 655392 | tf_op jit(solution)/shard_map/ppermute | solution.py:32
  226.7 6.8 %collective-permute-done.16 = f32[256,1]{0,1:T(1,128)S(1)} collective-permute-done((f32[256,1]{0,1:T(1,128)S(1)}, f32[256,1]{0,1:T(1,128)S(1)}, u32[]{:S(2)}, u32[]{:S(2)}) %collective-permute-start.16) | collective-permute-done | bytes 1056 | tf_op jit(solution)/shard_map/ppermute | solution.py:32
  233.5 1.0 fusion.24
  234.5 70.0 %all-reduce.4.cloned.1.call-done = (bf16[1024,1024]{1,0:T(8,128)(2,1)}, bf16[1024,1024]{1,0:T(8,128)(2,1)}) async-done(((bf16[1024,1024]{1,0:T(8,128)(2,1)}, bf16[1024,1024]{1,0:T(8,128)(2,1)}), (bf16[1024,1024]{1,0:T(8,128)(2,1)}, bf16[1024,1024]{1,0:T(8,128)(2,1)})) %all-reduce.4.cloned.1.call-update) | async-done | bytes 4194320 | tf_op jit(solution)/shard_map/psum | solution.py:1005
  304.5 4.1 %convert_element_type.94 = f32[1024,1024]{1,0:T(8,128)} convert(bf16[1024,1024]{1,0:T(8,128)(2,1)} %get-tuple-element.83) | non-fusion elementwise | flops 1048576 | bytes 6291456 | tf_op jit(solution)/shard_map/convert_element_type | solution.py:1089
  308.6 2.6 joined.4
  312.1 2.6 joined.5
  314.8 2.7 joined.6
  318.3 2.6 joined.7
  320.9 2.1 small_parts.1
  (127 shorter events, 21.2 us)
Async XLA Ops:
  7.2 31.7 %copy-start = (bf16[1024,1024]{1,0:T(8,128)(2,1)S(1)}, bf16[1024,1024]{1,0:T(8,128)(2,1)}, u32[]{:S(2)}) copy-start(bf16[1024,1024]{1,0:T(8,128)(2,1)} %param.23) | copy-start | bytes 6291460
  8.7 13.8 %collective-permute-start.1 = (bf16[16,512]{1,0:T(8,128)(2,1)}, bf16[16,512]{1,0:T(8,128)(2,1)S(1)}, u32[]{:S(2)}, u32[]{:S(2)}) collective-permute-start(bf16[16,512]{1,0:T(8,128)(2,1)} %edge_rows.1), channel_id=1, source_target_pairs={{0,2},{2,4},{4,6},{6,8},{8,10},{10,12},{12,14},{14,16},{16,18},{18... | collective-permute-start | bytes 49160 | tf_op jit(solution)/shard_map/ppermute | solution.py:27
  11.0 11.4 %collective-permute-start.2 = (bf16[16,512]{1,0:T(8,128)(2,1)}, bf16[16,512]{1,0:T(8,128)(2,1)S(1)}, u32[]{:S(2)}, u32[]{:S(2)}) collective-permute-start(bf16[16,512]{1,0:T(8,128)(2,1)} %edge_rows.1), channel_id=1, source_target_pairs={{0,3},{1,2},{2,5},{3,4},{4,7},{5,6},{6,9},{7,8},{8,11},{9,10},{10,... | collective-permute-start | bytes 49160 | tf_op jit(solution)/shard_map/ppermute | solution.py:50
  16.7 9.5 %collective-permute-start = (bf16[256,512]{1,0:T(8,128)(2,1)}, bf16[256,512]{1,0:T(8,128)(2,1)S(1)}, u32[]{:S(2)}, u32[]{:S(2)}) collective-permute-start(bf16[256,512]{1,0:T(8,128)(2,1)} %own_ref.1), channel_id=1, source_target_pairs={{0,1},{1,0},{2,3},{3,2},{4,5},{5,4},{6,7},{7,6},{8,9},{9,8},{10,11... | collective-permute-start | bytes 786440 | tf_op jit(solution)/shard_map/ppermute | solution.py:32
  17.3 20.8 %collective-permute-start.4 = (bf16[256,512]{1,0:T(8,128)(2,1)}, bf16[256,512]{1,0:T(8,128)(2,1)S(1)}, u32[]{:S(2)}, u32[]{:S(2)}) collective-permute-start(bf16[256,512]{1,0:T(8,128)(2,1)} %param.25), channel_id=1, source_target_pairs={{0,1},{1,0},{2,3},{3,2},{4,5},{5,4},{6,7},{7,6},{8,9},{9,8},{10,11... | collective-permute-start | bytes 786440 | tf_op jit(solution)/shard_map/ppermute | solution.py:32
  22.5 3.7 %copy-start.19 = (bf16[16,512]{1,0:T(8,128)(2,1)}, bf16[16,512]{1,0:T(8,128)(2,1)S(1)}, u32[]{:S(2)}) copy-start(bf16[16,512]{1,0:T(8,128)(2,1)S(1)} %collective-permute-done.1.edge_ref) | copy-start | bytes 49156
  22.5 3.7 %copy-start.20 = (bf16[16,512]{1,0:T(8,128)(2,1)}, bf16[16,512]{1,0:T(8,128)(2,1)S(1)}, u32[]{:S(2)}) copy-start(bf16[16,512]{1,0:T(8,128)(2,1)S(1)} %collective-permute-done.2.other_edge_ref) | copy-start | bytes 49156
  26.2 0.7 copy-start.15
  34.0 4.1 %copy-start.9 = (bf16[256,512]{1,0:T(8,128)(2,1)S(1)}, bf16[256,512]{1,0:T(8,128)(2,1)}, u32[]{:S(2)}) copy-start(bf16[256,512]{1,0:T(8,128)(2,1)} %param.25) | copy-start | bytes 786436
  37.5 4.9 %collective-permute-start.3 = (f32[96,256]{1,0:T(8,128)}, f32[96,256]{1,0:T(8,128)S(1)}, u32[]{:S(2)}, u32[]{:S(2)}) collective-permute-start(f32[96,256]{1,0:T(8,128)} %get-tuple-element.46.selected_ref), channel_id=1, source_target_pairs={{0,1},{1,0},{2,3},{3,2},{4,5},{5,4},{6,7},{7,6},{8,9},{9,8},{10,11... | collective-permute-start | bytes 294920 | tf_op jit(solution)/shard_map/ppermute | solution.py:32
  38.1 0.7 copy-start.4
  43.1 13.2 %copy-start.13 = (f32[16,1024]{1,0:T(8,128)S(1)}, f32[16,1024]{1,0:T(8,128)}, u32[]{:S(2)}) copy-start(f32[16,1024]{1,0:T(8,128)} %decay_log_ref.5) | copy-start | bytes 196612
  43.1 16.4 %copy-start.7 = (bf16[272,1024]{1,0:T(8,128)(2,1)S(1)}, bf16[272,1024]{1,0:T(8,128)(2,1)}, u32[]{:S(2)}) copy-start(bf16[272,1024]{1,0:T(8,128)(2,1)} %get-tuple-element.45) | copy-start | bytes 1671172
  53.9 1.7 collective-permute-start.5
  57.9 7.4 %collective-permute-start.6 = (f32[40,1024]{1,0:T(8,128)}, f32[40,1024]{1,0:T(8,128)}, u32[]{:S(2)}, u32[]{:S(2)}) collective-permute-start(f32[40,1024]{1,0:T(8,128)} %pad_maximum_fusion.8), channel_id=1, source_target_pairs={{0,4},{2,6},{4,0},{6,2},{8,12},{10,14},{12,8},{14,10},{16,20},{18,... | collective-permute-start | bytes 491528 | tf_op jit(solution)/shard_map/ppermute | solution.py:32
  59.6 12.4 %collective-permute-start.10 = (bf16[256,256]{1,0:T(8,128)(2,1)S(1)}, bf16[256,256]{1,0:T(8,128)(2,1)S(1)}, u32[]{:S(2)}, u32[]{:S(2)}) collective-permute-start(bf16[256,256]{1,0:T(8,128)(2,1)S(1)} %get-tuple-element.101), channel_id=1, source_target_pairs={{0,4},{2,6},{4,0},{6,2},{8,12},{10,14},{12,8},{14,10},{16,20},{18,... | collective-permute-start | bytes 393224 | tf_op jit(solution)/shard_map/ppermute | solution.py:32
  60.2 11.8 %collective-permute-start.11 = (bf16[256,256]{1,0:T(8,128)(2,1)S(1)}, bf16[256,256]{1,0:T(8,128)(2,1)S(1)}, u32[]{:S(2)}, u32[]{:S(2)}) collective-permute-start(bf16[256,256]{1,0:T(8,128)(2,1)S(1)} %get-tuple-element.100), channel_id=1, source_target_pairs={{0,2},{2,0},{4,6},{6,4},{8,10},{10,8},{12,14},{14,12},{16,18},{18,... | collective-permute-start | bytes 393224 | tf_op jit(solution)/shard_map/ppermute | solution.py:32
  60.2 11.8 %collective-permute-start.12 = (bf16[256,256]{1,0:T(8,128)(2,1)S(1)}, bf16[256,256]{1,0:T(8,128)(2,1)S(1)}, u32[]{:S(2)}, u32[]{:S(2)}) collective-permute-start(bf16[256,256]{1,0:T(8,128)(2,1)S(1)} %get-tuple-element.99), channel_id=1, source_target_pairs={{0,6},{2,4},{4,2},{6,0},{8,14},{10,12},{12,10},{14,8},{16,22},{18,... | collective-permute-start | bytes 393224 | tf_op jit(solution)/shard_map/ppermute | solution.py:32
  67.0 5.9 %collective-permute-start.7 = (f32[16,1024]{1,0:T(8,128)S(1)}, f32[16,1024]{1,0:T(8,128)S(1)}, u32[]{:S(2)}, u32[]{:S(2)}) collective-permute-start(f32[16,1024]{1,0:T(8,128)S(1)} %get-tuple-element.120), channel_id=1, source_target_pairs={{0,8},{2,10},{4,12},{6,14},{8,16},{10,18},{12,20},{14,22},{16,24},... | collective-permute-start | bytes 196616 | tf_op jit(solution)/shard_map/ppermute | solution.py:27
  70.5 6.2 %collective-permute-start.9 = (f32[16,1024]{1,0:T(8,128)S(1)}, f32[16,1024]{1,0:T(8,128)S(1)}, u32[]{:S(2)}, u32[]{:S(2)}) collective-permute-start(f32[16,1024]{1,0:T(8,128)S(1)} %get-tuple-element.119), channel_id=1, source_target_pairs={{8,0},{10,2},{12,4},{14,6},{16,8},{18,10},{20,12},{22,14},{24,16},... | collective-permute-start | bytes 196616 | tf_op jit(solution)/shard_map/ppermute | solution.py:27
  78.3 10.4 %copy-start.5 = (bf16[256,512]{1,0:T(8,128)(2,1)S(1)}, bf16[256,512]{1,0:T(8,128)(2,1)}, u32[]{:S(2)}) copy-start(bf16[256,512]{1,0:T(8,128)(2,1)} %copy-done.4) | copy-start | bytes 786436
  88.7 3.2 copy-start.1
  88.7 3.2 copy-start.8
  94.0 24.8 %copy-start.21 = (s32[256]{0:T(256)S(1)}, s32[256]{0:T(256)}, u32[]{:S(2)}) copy-start(s32[256]{0:T(256)} %ids_ref.1) | copy-start | bytes 3076
  118.1 186.4 %all-reduce.4.cloned.1.call-start = ((), (), s32[]{:S(2)}) async-start(), calls=%async_computation | async-start | bytes 8388608 | tf_op jit(solution)/shard_map/psum | solution.py:1005
  118.2 4.9 %collective-permute-start.13 = (f32[96,256]{1,0:T(8,128)}, f32[96,256]{1,0:T(8,128)S(1)}, u32[]{:S(2)}, u32[]{:S(2)}) collective-permute-start(f32[96,256]{1,0:T(8,128)} %get-tuple-element.52.select_grad_ref), channel_id=1, source_target_pairs={{0,1},{1,0},{2,3},{3,2},{4,5},{5,4},{6,7},{7,6},{8,9},{9,8},{10,11... | collective-permute-start | bytes 294920 | tf_op jit(solution)/shard_map/ppermute | solution.py:32
  123.1 0.6 copy-start.29
  123.7 7.2 %copy-start.16 = (f32[256,1]{1,0:T(8,128)S(1)}, f32[256,1]{1,0:T(8,128)}, u32[]{:S(2)}) copy-start(f32[256,1]{1,0:T(8,128)} %get-tuple-element.50) | copy-start | bytes 3076
  123.7 12.2 %copy-start.26 = (bf16[1024,2,1024]{2,1,0:T(2,128)(2,1)S(1)}, bf16[1024,2,1024]{2,1,0:T(2,128)(2,1)}, u32[]{:S(2)}) copy-start(bf16[1024,2,1024]{2,1,0:T(2,128)(2,1)} %param.15) | copy-start | bytes 12582916
  128.5 4.2 %copy-start.17 = (f32[16,1024]{1,0:T(8,128)S(1)}, f32[16,1024]{1,0:T(8,128)}, u32[]{:S(2)}) copy-start(f32[16,1024]{1,0:T(8,128)} %get-tuple-element.56) | copy-start | bytes 196612
  128.5 7.4 %slice-start = ((bf16[2,256,1024]{2,1,0:T(8,128)(2,1)}), bf16[1,256,1024]{2,1,0:T(8,128)(2,1)S(1)}, s32[]{:S(2)}) async-start(bf16[2,256,1024]{2,1,0:T(8,128)(2,1)} %scan_forward.1), calls=%async_computation.1 | async-start | bytes 1048576 | tf_op jit(solution)/shard_map/slice | solution.py:998
  128.5 7.4 %copy-start.18 = (f32[1024]{0:T(1024)S(1)}, f32[1024]{0:T(1024)}, u32[]{:S(2)}) copy-start(f32[1024]{0:T(1024)} %param.14) | copy-start | bytes 12292
  128.5 7.4 %copy-start.27 = (bf16[272,1024]{1,0:T(8,128)(2,1)S(1)}, bf16[272,1024]{1,0:T(8,128)(2,1)}, u32[]{:S(2)}) copy-start(bf16[272,1024]{1,0:T(8,128)(2,1)} %get-tuple-element.57) | copy-start | bytes 1671172
  129.4 3.3 %collective-permute-start.14 = (f32[8,1024]{1,0:T(8,128)S(1)}, f32[8,1024]{1,0:T(8,128)S(1)}, u32[]{:S(2)}, u32[]{:S(2)}) collective-permute-start(f32[8,1024]{1,0:T(8,128)S(1)} %slice.118), channel_id=1, source_target_pairs={{2,0},{4,2},{6,4},{8,6},{10,8},{12,10},{14,12},{16,14},{18,16},{20... | collective-permute-start | bytes 98312 | tf_op jit(solution)/shard_map/ppermute | solution.py:27
  131.6 7.7 %copy-start.22 = (f32[256]{0:T(256)}, f32[256]{0:T(256)S(1)}, u32[]{:S(2)}) copy-start(f32[256]{0:T(256)S(1)} %get-tuple-element.80) | copy-start | bytes 3076
  133.7 14.6 %collective-permute-start.17 = (bf16[256,1024]{1,0:T(8,128)(2,1)}, bf16[256,1024]{1,0:T(8,128)(2,1)}, u32[]{:S(2)}, u32[]{:S(2)}) collective-permute-start(bf16[256,1024]{1,0:T(8,128)(2,1)} %get-tuple-element.96.own_ref), channel_id=1, source_target_pairs={{0,4},{2,6},{4,0},{6,2},{8,12},{10,14},{12,8},{14,10},{16,20},{18,... | collective-permute-start | bytes 1572872 | tf_op jit(solution)/shard_map/ppermute | solution.py:32
  135.9 12.9 %copy-start.14 = (f32[96,1024]{1,0:T(8,128)S(1)}, f32[96,1024]{1,0:T(8,128)}, u32[]{:S(2)}) copy-start(f32[96,1024]{1,0:T(8,128)} %get-tuple-element.58) | copy-start | bytes 1179652
  139.3 3.6 %collective-permute-start.20 = (f32[1,1024]{1,0:T(1,128)S(1)}, f32[1,1024]{1,0:T(1,128)S(1)}, u32[]{:S(2)}, u32[]{:S(2)}) collective-permute-start(f32[1,1024]{1,0:T(1,128)S(1)} %bitcast.69), channel_id=1, source_target_pairs={{0,1},{1,0},{2,3},{3,2},{4,5},{5,4},{6,7},{7,6},{8,9},{9,8},{10,11... | collective-permute-start | bytes 12296 | tf_op jit(solution)/shard_map/ppermute | solution.py:32
  139.8 22.4 %collective-permute-start.18 = (bf16[256,1024]{1,0:T(8,128)(2,1)}, bf16[256,1024]{1,0:T(8,128)(2,1)}, u32[]{:S(2)}, u32[]{:S(2)}) collective-permute-start(bf16[256,1024]{1,0:T(8,128)(2,1)} %get-tuple-element.96.own_ref), channel_id=1, source_target_pairs={{0,2},{2,0},{4,6},{6,4},{8,10},{10,8},{12,14},{14,12},{16,18},{18,... | collective-permute-start | bytes 1572872 | tf_op jit(solution)/shard_map/ppermute | solution.py:32
  148.3 13.9 %collective-permute-start.19 = (bf16[256,1024]{1,0:T(8,128)(2,1)}, bf16[256,1024]{1,0:T(8,128)(2,1)}, u32[]{:S(2)}, u32[]{:S(2)}) collective-permute-start(bf16[256,1024]{1,0:T(8,128)(2,1)} %collective-permute-done.17.near_ref), channel_id=1, source_target_pairs={{0,2},{2,0},{4,6},{6,4},{8,10},{10,8},{12,14},{14,12},{16,18},{18,... | collective-permute-start | bytes 1572872 | tf_op jit(solution)/shard_map/ppermute | solution.py:32
  150.0 1.0 copy-start.3
  151.7 2.5 collective-permute-start.21
  151.8 7.0 %collective-permute-start.22 = (bf16[64,1024]{1,0:T(8,128)(2,1)}, bf16[64,1024]{1,0:T(8,128)(2,1)S(1)}, u32[]{:S(2)}, u32[]{:S(2)}) collective-permute-start(bf16[64,1024]{1,0:T(8,128)(2,1)} %get-tuple-element.93), channel_id=1, source_target_pairs={{0,4},{2,6},{4,0},{6,2},{8,12},{10,14},{12,8},{14,10},{16,20},{18,... | collective-permute-start | bytes 393224 | tf_op jit(solution)/shard_map/ppermute | solution.py:32
  154.2 6.3 %collective-permute-start.23 = (bf16[64,1024]{1,0:T(8,128)(2,1)}, bf16[64,1024]{1,0:T(8,128)(2,1)S(1)}, u32[]{:S(2)}, u32[]{:S(2)}) collective-permute-start(bf16[64,1024]{1,0:T(8,128)(2,1)} %get-tuple-element.92), channel_id=1, source_target_pairs={{0,6},{2,4},{4,2},{6,0},{8,14},{10,12},{12,10},{14,8},{16,22},{18,... | collective-permute-start | bytes 393224 | tf_op jit(solution)/shard_map/ppermute | solution.py:32
  166.7 9.5 %collective-permute-start.24 = (bf16[80,1024]{1,0:T(8,128)(2,1)S(1)}, bf16[80,1024]{1,0:T(8,128)(2,1)S(1)}, u32[]{:S(2)}, u32[]{:S(2)}) collective-permute-start(bf16[80,1024]{1,0:T(8,128)(2,1)S(1)} %get-tuple-element.104), channel_id=1, source_target_pairs={{0,8},{2,10},{4,12},{6,14},{8,0},{10,2},{12,4},{14,6},{16,24},{18,... | collective-permute-start | bytes 491528 | tf_op jit(solution)/shard_map/ppermute | solution.py:32
  168.2 15.0 %collective-permute-start.25 = (bf16[80,1024]{1,0:T(8,128)(2,1)S(1)}, bf16[80,1024]{1,0:T(8,128)(2,1)S(1)}, u32[]{:S(2)}, u32[]{:S(2)}) collective-permute-start(bf16[80,1024]{1,0:T(8,128)(2,1)S(1)} %get-tuple-element.106), channel_id=1, source_target_pairs={{0,16},{2,18},{4,20},{6,22},{8,24},{10,26},{12,28},{14,30},{16,0},... | collective-permute-start | bytes 491528 | tf_op jit(solution)/shard_map/ppermute | solution.py:32
  168.8 14.4 %collective-permute-start.26 = (bf16[80,1024]{1,0:T(8,128)(2,1)S(1)}, bf16[80,1024]{1,0:T(8,128)(2,1)S(1)}, u32[]{:S(2)}, u32[]{:S(2)}) collective-permute-start(bf16[80,1024]{1,0:T(8,128)(2,1)S(1)} %get-tuple-element.105), channel_id=1, source_target_pairs={{0,24},{2,26},{4,28},{6,30},{8,16},{10,18},{12,20},{14,22},{16,8},... | collective-permute-start | bytes 491528 | tf_op jit(solution)/shard_map/ppermute | solution.py:32
  184.3 9.1 %collective-permute-start.29 = (bf16[80,1024]{1,0:T(8,128)(2,1)S(1)}, bf16[80,1024]{1,0:T(8,128)(2,1)S(1)}, u32[]{:S(2)}, u32[]{:S(2)}) collective-permute-start(bf16[80,1024]{1,0:T(8,128)(2,1)S(1)} %add_convert_fusion), channel_id=1, source_target_pairs={{0,8},{2,10},{4,12},{6,14},{8,0},{10,2},{12,4},{14,6},{16,24},{18,... | collective-permute-start | bytes 491528 | tf_op jit(solution)/shard_map/ppermute | solution.py:32
  187.8 13.9 %collective-permute-start.27 = (bf16[80,1024]{1,0:T(8,128)(2,1)S(1)}, bf16[80,1024]{1,0:T(8,128)(2,1)S(1)}, u32[]{:S(2)}, u32[]{:S(2)}) collective-permute-start(bf16[80,1024]{1,0:T(8,128)(2,1)S(1)} %add_convert_fusion), channel_id=1, source_target_pairs={{0,24},{2,26},{4,28},{6,30},{8,16},{10,18},{12,20},{14,22},{16,8},... | collective-permute-start | bytes 491528 | tf_op jit(solution)/shard_map/ppermute | solution.py:32
  190.0 16.8 %collective-permute-start.28 = (bf16[80,1024]{1,0:T(8,128)(2,1)S(1)}, bf16[80,1024]{1,0:T(8,128)(2,1)S(1)}, u32[]{:S(2)}, u32[]{:S(2)}) collective-permute-start(bf16[80,1024]{1,0:T(8,128)(2,1)S(1)} %add_convert_fusion), channel_id=1, source_target_pairs={{0,16},{2,18},{4,20},{6,22},{8,24},{10,26},{12,28},{14,30},{16,0},... | collective-permute-start | bytes 491528 | tf_op jit(solution)/shard_map/ppermute | solution.py:32
  207.9 5.6 %copy-start.2 = (f32[256,1024]{1,0:T(8,128)S(1)}, f32[256,1024]{1,0:T(8,128)}, u32[]{:S(2)}) copy-start(f32[256,1024]{1,0:T(8,128)} %get-tuple-element.130) | copy-start | bytes 3145732
  207.9 18.8 %collective-permute-start.30 = (bf16[320,1024]{1,0:T(8,128)(2,1)}, bf16[320,1024]{1,0:T(8,128)(2,1)}, u32[]{:S(2)}, u32[]{:S(2)}) collective-permute-start(bf16[320,1024]{1,0:T(8,128)(2,1)} %pad_maximum_fusion.inner_ref), channel_id=1, source_target_pairs={{0,4},{2,6},{4,0},{6,2},{8,12},{10,14},{12,8},{14,10},{16,20},{18,... | collective-permute-start | bytes 1966088 | tf_op jit(solution)/shard_map/ppermute | solution.py:32
  212.7 2.4 copy-start.25
  212.7 20.8 %copy-start.6 = (bf16[256,512]{1,0:T(8,128)(2,1)S(1)}, bf16[256,512]{1,0:T(8,128)(2,1)}, u32[]{:S(2)}) copy-start(bf16[256,512]{1,0:T(8,128)(2,1)} %own_ref.1) | copy-start | bytes 786436
  212.7 20.8 %copy-start.10 = (bf16[256,512]{1,0:T(8,128)(2,1)S(1)}, bf16[256,512]{1,0:T(8,128)(2,1)}, u32[]{:S(2)}) copy-start(bf16[256,512]{1,0:T(8,128)(2,1)} %param.25) | copy-start | bytes 786436
  212.7 20.8 %copy-start.23 = (f32[256]{0:T(256)S(1)}, f32[256]{0:T(256)}, u32[]{:S(2)}) copy-start(f32[256]{0:T(256)} %copy-done.22) | copy-start | bytes 3076
  212.7 20.8 %copy-start.24 = (f32[256]{0:T(256)S(1)}, f32[256]{0:T(256)}, u32[]{:S(2)}) copy-start(f32[256]{0:T(256)} %get-tuple-element.81) | copy-start | bytes 3076
  212.8 20.6 %collective-permute-start.8 = (f32[256,512]{1,0:T(8,128)S(1)}, f32[256,512]{1,0:T(8,128)S(1)}, u32[]{:S(2)}, u32[]{:S(2)}) collective-permute-start(f32[256,512]{1,0:T(8,128)S(1)} %slice_select_fusion.1), channel_id=1, source_target_pairs={{0,1},{1,0},{2,3},{3,2},{4,5},{5,4},{6,7},{7,6},{8,9},{9,8},{10,11... | collective-permute-start | bytes 1572872 | tf_op jit(solution)/shard_map/ppermute | solution.py:32
  213.5 20.0 %collective-permute-start.15 = (f32[256,512]{1,0:T(8,128)S(1)}, f32[256,512]{1,0:T(8,128)S(1)}, u32[]{:S(2)}, u32[]{:S(2)}) collective-permute-start(f32[256,512]{1,0:T(8,128)S(1)} %slice_select_fusion), channel_id=1, source_target_pairs={{0,1},{1,0},{2,3},{3,2},{4,5},{5,4},{6,7},{7,6},{8,9},{9,8},{10,11... | collective-permute-start | bytes 1572872 | tf_op jit(solution)/shard_map/ppermute | solution.py:32
  215.1 18.4 %collective-permute-start.16 = (f32[256,1]{0,1:T(1,128)S(1)}, f32[256,1]{0,1:T(1,128)S(1)}, u32[]{:S(2)}, u32[]{:S(2)}) collective-permute-start(f32[256,1]{0,1:T(1,128)S(1)} %bitcast.75), channel_id=1, source_target_pairs={{0,1},{1,0},{2,3},{3,2},{4,5},{5,4},{6,7},{7,6},{8,9},{9,8},{10,11... | collective-permute-start | bytes 3080 | tf_op jit(solution)/shard_map/ppermute | solution.py:32
  215.6 95.7 %collective-permute-start.32 = (bf16[320,1024]{1,0:T(8,128)(2,1)}, bf16[320,1024]{1,0:T(8,128)(2,1)S(1)}, u32[]{:S(2)}, u32[]{:S(2)}) collective-permute-start(bf16[320,1024]{1,0:T(8,128)(2,1)} %pad_maximum_fusion.inner_ref), channel_id=1, source_target_pairs={{0,2},{2,0},{4,6},{6,4},{8,10},{10,8},{12,14},{14,12},{16,18},{18,... | collective-permute-start | bytes 1966088 | tf_op jit(solution)/shard_map/ppermute | solution.py:32
  226.7 90.8 %collective-permute-start.31 = (bf16[320,1024]{1,0:T(8,128)(2,1)}, bf16[320,1024]{1,0:T(8,128)(2,1)S(1)}, u32[]{:S(2)}, u32[]{:S(2)}) collective-permute-start(bf16[320,1024]{1,0:T(8,128)(2,1)} %collective-permute-done.30.inner_ref), channel_id=1, source_target_pairs={{0,2},{2,0},{4,6},{6,4},{8,10},{10,8},{12,14},{14,12},{16,18},{18,... | collective-permute-start | bytes 1966088 | tf_op jit(solution)/shard_map/ppermute | solution.py:32
  311.3 0.9 copy-start.12
  317.4 0.9 copy-start.11
  (1 other events, 0.6 us)
Sparse Core Ops, SparseCore 0:
  188.0 116.5 all-reduce.3

commit v7 on v6

--- a/solution.py
+++ b/solution.py
@@ -15,6 +15,7 @@
 body_rows = 32
 scan_width = 512
 vmem_bytes = 56 * 1024 * 1024
+tiny_cost = pl.CostEstimate(flops=1, bytes_accessed=1, transcendentals=0)
 f32 = jnp.float32
 bf16 = jnp.bfloat16
 contract_first = (((0,), (0,)), ((), ()))
@@ -124,8 +125,7 @@
     return pl.BlockSpec((rows, width), lambda j: (0, 0))
 
 
-def call(kernel, name, width, in_specs, out_specs, out_shape, scratch, flops, *operands):
-    moved = sum(a.size * a.dtype.itemsize for a in operands)
+def call(kernel, name, width, in_specs, out_specs, out_shape, scratch, *operands):
     return pl.pallas_call(
         kernel,
         grid=(width // scan_width,),
@@ -134,7 +134,7 @@
         out_shape=out_shape,
         scratch_shapes=scratch,
         compiler_params=pltpu.CompilerParams(vmem_limit_bytes=vmem_bytes),
-        cost_estimate=pl.CostEstimate(flops=flops, bytes_accessed=moved, transcendentals=0),
+        cost_estimate=tiny_cost,
         name=name,
     )(*operands)
 
@@ -195,7 +195,6 @@
             jax.ShapeDtypeStruct((columns, rows), f32),
         ],
         [pltpu.VMEM((extended, scan_width), f32)],
-        4_000_000_000,
         projected,
         conv_weight,
         conv_bias,
@@ -296,7 +295,6 @@
             jax.ShapeDtypeStruct((2 * count + 8, width), f32),
         ],
         [pltpu.VMEM((2 * count, rows), f32)] + [pltpu.VMEM((rows, scan_width), f32)] * 3,
-        10_000_000_000,
         selected,
         other,
         step_weight,
@@ -421,7 +419,6 @@
         [pltpu.VMEM((2 * count, rows), f32)]
         + [pltpu.VMEM((rows, scan_width), f32)] * 3
         + [pltpu.VMEM((8 * body_rows * (scan_width // lanes), lanes), f32)],
-        10_000_000_000,
         selected,
         other,
         step,
@@ -610,7 +607,6 @@
             pltpu.VMEM((rows * count, lanes), f32),
             pltpu.VMEM((rows * count, lanes), f32),
         ],
-        22_000_000_000,
         selected,
         other,
         step_pre,
@@ -711,7 +707,6 @@
             jax.ShapeDtypeStruct((small, width), f32),
         ],
         [pltpu.VMEM((extended, scan_width), f32), pltpu.VMEM((rows + 16, scan_width), f32)],
-        5_000_000_000,
         select_grad,
         other,
         select_weight,
@@ -749,6 +744,7 @@
             jax.ShapeDtypeStruct((extended, 2 * half), bf16),
             jax.ShapeDtypeStruct((rows, 1), f32),
         ],
+        cost_estimate=tiny_cost,
         name="normalized",
     )(own, other, edge, other_edge, gain)
 
@@ -776,6 +772,7 @@
         ],
         out_specs=pl.BlockSpec((halo, width), lambda j: (0, 0)),
         out_shape=jax.ShapeDtypeStruct((halo, width), bf16),
+        cost_estimate=tiny_cost,
         name="edge_rows",
     )(ids, tokens)
 
@@ -815,9 +812,7 @@
         ],
         scratch_shapes=[pltpu.VMEM((quarter, width), f32)],
         compiler_params=pltpu.CompilerParams(vmem_limit_bytes=vmem_bytes),
-        cost_estimate=pl.CostEstimate(
-            flops=2_000_000_000, bytes_accessed=4_000_000, transcendentals=0
-        ),
+        cost_estimate=tiny_cost,
         name="inner_quarter",
     )(place, own, near, far, last, normed, small)
 
@@ -861,6 +856,7 @@
         ],
         input_output_aliases={3 + k: k for k in range(len(before))},
         compiler_params=pltpu.CompilerParams(vmem_limit_bytes=vmem_bytes),
+        cost_estimate=tiny_cost,
         name="joined",
     )(place, gate, inner, *untouched)
 
@@ -875,6 +871,7 @@
     return pl.pallas_call(
         functools.partial(parts_kernel, starts=[start for start, _ in sizes]),
         out_shape=[jax.ShapeDtypeStruct((rows, width), f32) for _, rows in sizes],
+        cost_estimate=tiny_cost,
         name="small_parts",
     )(small)
 
@@ -1003,23 +1000,82 @@
         lax.dot_general(normed, gate_grad, contract_first, preferred_element_type=f32).astype(bf16),
     )
     out_sum, gate_sum = lax.psum(products, "wide")
-    act_grad, select_grad, scan_small = scan_backward(
-        selected,
-        other_selected,
-        step_pre,
-        step,
-        act,
-        projected,
-        gated_grad,
-        masks,
-        decay_log,
-        entry,
-        tail,
-        skip_gain[None],
-        step_weight,
-        [normed_four, *products],
-    )
-    other_select_grad = swapped(select_grad, "narrow", 1)
+    whole = whole_ext[:rows].astype(f32)
+    wide_place = lax.axis_index("wide").astype(jnp.int32)
+
+    def after_forward(pair):
+        act_grad, select_grad, scan_small = scan_backward(
+            selected,
+            other_selected,
+            step_pre,
+            step,
+            act,
+            projected,
+            gated_grad,
+            masks,
+            decay_log,
+            entry,
+            tail,
+            skip_gain[None],
+            step_weight,
+            [normed_four, *products],
+        )
+        other_select_grad = swapped(select_grad, "narrow", 1)
+
+        inner_main, edges, conv_small = convolve_grad(
+            select_grad,
+            other_select_grad,
+            select_weight,
+            act_grad,
+            convolved,
+            act,
+            projected,
+            conv_weight,
+            masks,
+        )
+        from_next = passed_along(edges[:8], "wide", -1)
+        last_rows = edges[8:] + jnp.where(same_as_last, from_next, 0.0)
+        inner_grad = jnp.concatenate([inner_main[: rows - 8], last_rows.astype(bf16)])
+        normed_part = jnp.einsum(
+            "cte,dce->td", jnp.stack([inner_grad, gate_grad]), in_weight, preferred_element_type=f32
+        )
+        gain_part = jnp.sum(normed_part * whole * inverse, axis=0, keepdims=True)
+        row_part = jnp.sum(normed_part * norm_gain * whole, axis=1, keepdims=True)
+
+        gain_sum = gain_part + swapped(gain_part, "narrow", 1)
+        spare = -(scan_small.shape[0] + conv_small.shape[0] + 1) % 256
+        small = jnp.concatenate(
+            [scan_small, conv_small, gain_sum, jnp.zeros((spare, gain_sum.shape[1]), f32)]
+        )
+        small_piece = scattered(small, (1, 2))
+        near = swapped(inner_grad, "wide", 2)
+        keep, sends = inner_quarter(
+            (wide_place >> 2 & 3)[None],
+            inner_grad,
+            near,
+            swapped(inner_grad, "wide", 1),
+            swapped(near, "wide", 1),
+            normed_four,
+            small_piece,
+        )
+        first_bits, *more_bits = group_bits(2)
+        held = keep
+        for n, flip in enumerate(flips(first_bits)[1:]):
+            held = held + swapped(sends[n], "wide", flip).astype(f32)
+        for bits in more_bits:
+            held = scattered(held, bits)
+        held = held.astype(bf16)
+        for bits in reversed(group_bits(2)):
+            held = gathered(held, bits)
+        return held, normed_part, row_part
+
+    kinds = jax.eval_shape(after_forward, pair)
+    held, normed_part, row_part = lax.cond(
+        segment_ids[0] >= 0,
+        after_forward,
+        lambda pair: jax.tree.map(lambda kind: jnp.zeros(kind.shape, kind.dtype), kinds),
+        pair,
+    )
 
     def narrow_halves(array):
         low, high = array[:, :features], array[:, features:]
@@ -1030,53 +1086,6 @@
     out_total = out_mine + swapped(out_other, "narrow", 1)
     layer_out = (tokens.astype(f32) + out_total).astype(bf16)
 
-    inner_main, edges, conv_small = convolve_grad(
-        select_grad,
-        other_select_grad,
-        select_weight,
-        act_grad,
-        convolved,
-        act,
-        projected,
-        conv_weight,
-        masks,
-    )
-    from_next = passed_along(edges[:8], "wide", -1)
-    last_rows = edges[8:] + jnp.where(same_as_last, from_next, 0.0)
-    inner_grad = jnp.concatenate([inner_main[: rows - 8], last_rows.astype(bf16)])
-    normed_part = jnp.einsum(
-        "cte,dce->td", jnp.stack([inner_grad, gate_grad]), in_weight, preferred_element_type=f32
-    )
-    whole = whole_ext[:rows].astype(f32)
-    gain_part = jnp.sum(normed_part * whole * inverse, axis=0, keepdims=True)
-    row_part = jnp.sum(normed_part * norm_gain * whole, axis=1, keepdims=True)
-
-    gain_sum = gain_part + swapped(gain_part, "narrow", 1)
-    spare = -(scan_small.shape[0] + conv_small.shape[0] + 1) % 256
-    small = jnp.concatenate(
-        [scan_small, conv_small, gain_sum, jnp.zeros((spare, gain_sum.shape[1]), f32)]
-    )
-    small_piece = scattered(small, (1, 2))
-    near = swapped(inner_grad, "wide", 2)
-    wide_place = lax.axis_index("wide").astype(jnp.int32)
-    keep, sends = inner_quarter(
-        (wide_place >> 2 & 3)[None],
-        inner_grad,
-        near,
-        swapped(inner_grad, "wide", 1),
-        swapped(near, "wide", 1),
-        normed_four,
-        small_piece,
-    )
-    first_bits, *more_bits = group_bits(2)
-    held = keep
-    for n, flip in enumerate(flips(first_bits)[1:]):
-        held = held + swapped(sends[n], "wide", flip).astype(f32)
-    for bits in more_bits:
-        held = scattered(held, bits)
-    held = held.astype(bf16)
-    for bits in reversed(group_bits(2)):
-        held = gathered(held, bits)
     normed_mine, normed_other = narrow_halves(normed_part)
     row_sum = row_part + swapped(row_part, "narrow", 1)
     normed_sum = normed_mine + swapped(normed_other, "narrow", 1)
@@ -1100,8 +1109,8 @@
             [layer_out, tokens_grad] if flip == 1 else [],
         )
     in_weight_grad, small_sum = results
-    conv_at = scan_small.shape[0]
-    gain_at = conv_at + conv_small.shape[0]
+    conv_at = rank + count + 16
+    gain_at = conv_at + columns + 16
     (
         step_weight_grad,
         decay_log_grad,

time: 331 us -> 285 us (0.86)
  waiting for transfers between devices: 149 us -> 86.9 us
  other arithmetic: 20.8 us -> 31.6 us
  local copies, waits for them, and re-layouts: 11.6 us -> 18.9 us
    psum x1, waiting for transfers between devices: 70 us -> 0.01 us  [local(): out_sum, gate_sum = lax.psum(products, 'wide')]
    ppermute x28, waiting for transfers between devices: 75 us -> 82.7 us  [swapped(): return lax.ppermute(array, axis, [(i, i ^ bit) for i in range(peers)])]
    slice x2 -> x4, local copies, waits for them, and re-layouts: 1.92 us -> 5.36 us  [the longest x1 2.27 us: narrow_halves(): low, high = (array[:, :features], array[:, features:])]
  transfers between devices with their start and end apart: 34 -> 34, of which waited for: 18 -> 17; matrix products, arithmetic and copies ran while one was open for 9% -> 20% of each run, Pallas kernels for 4% -> 20%
where the time goes in v7:
time: 285 us; the launch traced here: 283 us
  waiting for transfers between devices  86.9 us (30%)
  Pallas kernels  70.9 us (25%)
  starting transfers between devices  42 us (15%)
  other arithmetic  31.6 us (11%)
  local copies, waits for them, and re-layouts  18.9 us (7%)
  matrix products  17.5 us (6%)
  between operations  15.2 us (5%)
    ppermute x28, waiting for transfers between devices, swapped(): return lax.ppermute(array, axis, [(i, i ^ bit) for i in range(peers)])  82.7 us
    pallas_call x5, Pallas kernels, call(): pl.pallas_call(kernel, grid=(width // scan_width,), in_specs=in_specs, ou...  51.2 us
    ppermute x28, starting transfers between devices, swapped(): return lax.ppermute(array, axis, [(i, i ^ bit) for i in range(peers)])  30.2 us
    pallas_call x4, Pallas kernels, joined(): pl.pallas_call(join_kernel, grid_spec=pltpu.PrefetchScalarGridSpec(num_sc...  10.7 us
    ppermute x4, starting transfers between devices, passed_along(): return lax.ppermute(array, axis, pairs)  7.64 us
    dot_general x1, matrix products, after_forward(): jnp.einsum('cte,dce->td', jnp.stack([inner_grad, gate_grad]), in_weight,...  5.85 us
  transfers between devices with their start and end apart: 34, of which 17 were waited for; matrix products, arithmetic and copies ran while one was open for 20% of the time, Pallas kernels for 20%

profile of v7, /device:TPU:0, one launch (start us, length us, event | category | flops | bytes accessed | tf_op | source)
XLA Modules:
  0.0 283.3 jit_solution(5006416098539402079)
XLA Ops:
  7.2 3.0 %collective-permute-start.15 = (bf16[256,512]{1,0:T(8,128)(2,1)}, bf16[256,512]{1,0:T(8,128)(2,1)S(1)}, u32[]{:S(2)}, u32[]{:S(2)}) collective-permute-start(bf16[256,512]{1,0:T(8,128)(2,1)} %own_ref.1), channel_id=1, source_target_pairs={{0,1},{1,0},{2,3},{3,2},{4,5},{5,4},{6,7},{7,6},{8,9},{9,8},{10,11... | collective-permute-start | bytes 786440 | tf_op jit(solution)/shard_map/ppermute | solution.py:33
  10.3 1.4 edge_rows.1
  11.6 1.4 collective-permute-start.16
  13.1 4.1 %collective-permute-start.17 = (bf16[16,512]{1,0:T(8,128)(2,1)}, bf16[16,512]{1,0:T(8,128)(2,1)S(1)}, u32[]{:S(2)}, u32[]{:S(2)}) collective-permute-start(bf16[16,512]{1,0:T(8,128)(2,1)} %edge_rows.1), channel_id=1, source_target_pairs={{0,3},{1,2},{2,5},{3,4},{4,7},{5,6},{6,9},{7,8},{8,11},{9,10},{10,... | collective-permute-start | bytes 49160 | tf_op jit(solution)/shard_map/ppermute | solution.py:51
  17.2 1.5 collective-permute-start.19
  18.8 1.2 slice.101
  20.0 1.5 compare_convert_fusion
  23.1 2.2 normalized.1
  25.3 4.0 %fusion.21.inner_ref.gate_ref = bf16[2,272,1024]{2,1,0:T(8,128)(2,1)S(1)} fusion(bf16[1024,2,1024]{2,1,0:T(2,128)(2,1)} %param.17, bf16[272,1024]{1,0:T(8,128)(2,1)} %get-tuple-element.129), kind=kOutput, calls=%fused_computation.47 | convolution fusion | flops 1141407744 | bytes 5865472 | tf_op jit(solution)/shard_map/td,dce->cte/dot_general | solution.py:960
  29.3 3.3 %convolve.1 = (f32[256,1024]{1,0:T(8,128)}, bf16[256,1024]{1,0:T(8,128)(2,1)S(1)}, f32[96,256]{1,0:T(8,128)S(1)}) custom-call(bf16[2,272,1024]{2,1,0:T(8,128)(2,1)S(1)} %fusion.21.inner_ref.gate_ref, f32[4,1024]{1,0:T(4,128)S(1)} %copy-done.43, f32[1,1024]{1,0:T(1,128)} %bitcast.70, bf16[96,1024]{1,0:T(8,128)(2,1)S(1)} %copy-done.27, f32[256,8]{1,0:T(8,128)} %copy.41.mask_ref), custom_call_target="tpu_custom_call" | custom-call | flops 1 | bytes 1 | tf_op jit(solution)/shard_map/convolve/pallas_call | solution.py:129
  34.9 2.2 collective-permute-done.18.other_ref
  37.2 10.3 %scan_ends.1 = (f32[256,1024]{1,0:T(8,128)}, f32[256,1024]{1,0:T(8,128)}, f32[40,1024]{1,0:T(8,128)}) custom-call(f32[96,256]{1,0:T(8,128)S(1)} %get-tuple-element.130.selected_ref, f32[96,256]{1,0:T(8,128)S(1)} %collective-permute-done.18.other_ref, bf16[64,1024]{1,0:T(8,128)(2,1)S(1)} %copy-done.35, f32[1,1024]{1,0:T(1,128)} %bitcast.71, ...), custom_call_target="tpu_custom_call" | custom-call | flops 1 | bytes 1 | tf_op jit(solution)/shard_map/scan_ends/pallas_call | solution.py:129
  47.6 1.7 collective-permute-done.20
  52.4 1.6 collective-permute-start.21
  54.7 1.2 slice.119
  55.9 3.1 %collective-permute-done.21 = f32[40,1024]{1,0:T(8,128)} collective-permute-done((f32[40,1024]{1,0:T(8,128)}, f32[40,1024]{1,0:T(8,128)}, u32[]{:S(2)}, u32[]{:S(2)}) %collective-permute-start.21) | collective-permute-done | bytes 163872 | tf_op jit(solution)/shard_map/ppermute | solution.py:33
  59.0 1.4 fusion.34
  61.3 3.5 %collective-permute-start.22 = (f32[16,1024]{1,0:T(8,128)S(1)}, f32[16,1024]{1,0:T(8,128)S(1)}, u32[]{:S(2)}, u32[]{:S(2)}) collective-permute-start(f32[16,1024]{1,0:T(8,128)S(1)} %multiply_add_fusion.2), channel_id=1, source_target_pairs={{0,8},{2,10},{4,12},{6,14},{8,16},{10,18},{12,20},{14,22},{16,24},... | collective-permute-start | bytes 196616 | tf_op jit(solution)/shard_map/ppermute | solution.py:28
  65.6 1.5 collective-permute-start.25
  67.7 1.7 multiply_add_fusion
  69.5 9.7 %scan_forward.1 = bf16[2,256,1024]{2,1,0:T(8,128)(2,1)} custom-call(f32[96,256]{1,0:T(8,128)S(1)} %copy-done.22, f32[96,256]{1,0:T(8,128)S(1)} %copy-done.25, f32[256,1024]{1,0:T(8,128)S(1)} %copy-done.10, bf16[256,1024]{1,0:T(8,128)(2,1)S(1)} %copy-done.7, bf16[2,272,1024]{2,1,0:T(8,128)(2,1)S(1)} %fusion.21.inner_ref.gate_ref, f32[256,1024]{1,0:T(8,128)S(1)} %copy-done.2, ...), custom_call_target="tpu_custom_call" | custom-call | flops 1 | bytes 1 | tf_op jit(solution)/shard_map/scan_forward/pallas_call | solution.py:129
  79.2 3.2 %convolution_convert_fusion = bf16[1024,1024]{1,0:T(8,128)(2,1)} fusion(bf16[2,256,1024]{2,1,0:T(8,128)(2,1)} %scan_forward.1, bf16[272,1024]{1,0:T(8,128)(2,1)S(1)} %copy-done.17), kind=kOutput, calls=%fused_computation.44 | convolution fusion | flops 537919488 | bytes 3145728 | tf_op jit(solution)/shard_map/dot_general | solution.py:1000
  82.4 2.1 convolution_convert_fusion.1
  84.6 2.2 slice_convert_fusion
  86.8 1.9 pad_maximum_fusion.5
  88.7 1.4 collective-permute-start.24
  90.2 1.7 fusion.31
  92.7 4.2 %collective-permute-done.24 = f32[16,1024]{1,0:T(8,128)} collective-permute-done((f32[16,1024]{1,0:T(8,128)S(1)}, f32[16,1024]{1,0:T(8,128)}, u32[]{:S(2)}, u32[]{:S(2)}) %collective-permute-start.24) | collective-permute-done | bytes 65568 | tf_op jit(solution)/shard_map/ppermute | solution.py:28
  99.4 129.5 %conditional.1 = (bf16[320,1024]{1,0:T(8,128)(2,1)}, f32[256,1024]{1,0:T(8,128)}, f32[256,1]{0,1:T(1,128)}, f32[256,512]{1,0:T(8,128)}, f32[256,512]{1,0:T(8,128)}) conditional(s32[]{:T(128)} %convert_element_type.79, () %tuple.18, (s32[]{:T(128)}, f32[1024]{0:T(1024)}, f32[96,256]{1,0:T(8,128)S(1)}, f32[96,256]{1,0:T(8,128)S(1)}, ...), branch_computations={%region_0.1_spmd, %region_1.4_spmd} | conditional | flops 1082092288 | bytes 54264648 | solution.py:1073
  101.1 1.7 fusion.11.tail_ref
  102.8 23.9 %scan_backward.1 = (f32[256,1024]{1,0:T(8,128)}, f32[96,256]{1,0:T(8,128)}, f32[96,1024]{1,0:T(8,128)}) custom-call(f32[96,256]{1,0:T(8,128)S(1)} %get-tuple-element.55.selected_ref, f32[96,256]{1,0:T(8,128)S(1)} %get-tuple-element.56.other_ref, f32[256,1024]{1,0:T(8,128)} %get-tuple-element.57.step_pre_ref, f32[256,1024]{1,0:T(8,128)} %get-tuple-element.58.step_ref, ...), custom_call_target="tpu_custom_call" | custom-call | flops 1 | bytes 1 | tf_op jit(solution)/shard_map/cond/branch_1_fun/scan_backward/pallas_call | solution.py:129
  127.8 3.8 %collective-permute-done.other_ref = f32[96,256]{1,0:T(8,128)S(1)} collective-permute-done((f32[96,256]{1,0:T(8,128)}, f32[96,256]{1,0:T(8,128)S(1)}, u32[]{:S(2)}, u32[]{:S(2)}) %collective-permute-start) | collective-permute-done | bytes 98336 | tf_op jit(solution)/shard_map/cond/branch_1_fun/ppermute | solution.py:33
  132.2 4.1 %convolve_grad.1 = (bf16[256,1024]{1,0:T(8,128)(2,1)}, f32[16,1024]{1,0:T(8,128)}, f32[112,1024]{1,0:T(8,128)}) custom-call(f32[96,256]{1,0:T(8,128)} %get-tuple-element.71.select_grad_ref, f32[96,256]{1,0:T(8,128)} %copy-done.42, bf16[96,1024]{1,0:T(8,128)(2,1)S(1)} %copy-done.28, f32[256,1024]{1,0:T(8,128)} %get-tuple-element.73.act_grad_ref, ...), custom_call_target="tpu_custom_call" | custom-call | flops 1 | bytes 1 | tf_op jit(solution)/shard_map/cond/branch_1_fun/convolve_grad/pallas_call | solution.py:129
  137.1 1.3 collective-permute-start.1
  141.3 2.2 collective-permute-start.2
  143.5 5.8 %multiply_reduce_fusion = (f32[256]{0:T(256)}, f32[1024]{0:T(1024)S(1)}, f32[256,1024]{1,0:T(8,128)}) fusion(f32[256,1024]{1,0:T(8,128)} %get-tuple-element.83, f32[1024]{0:T(1024)S(1)} %copy-done.47, f32[256]{0:T(256)S(1)} %bitcast.78, bf16[1024,2,1024]{2,1,0:T(2,128)(2,1)} %get-tuple-element.301, bf16[1,256,1024]{2,1,0:T(8,128)(2,1)S(1)} %copy-done.36, ...), kind=kOutput, calls=%fused_computation.7 | convolution fusion | flops 1075837696 | bytes 7350272 | tf_op jit(solution)/shard_map/cond/branch_1_fun/cte,dce->td/dot_general | solution.py:1039
  150.7 2.3 collective-permute-done.5
  153.0 6.4 %collective-permute-done.2.near_ref = bf16[256,1024]{1,0:T(8,128)(2,1)} collective-permute-done((bf16[256,1024]{1,0:T(8,128)(2,1)S(1)}, bf16[256,1024]{1,0:T(8,128)(2,1)}, u32[]{:S(2)}, u32[]{:S(2)}) %collective-permute-start.2) | collective-permute-done | bytes 524320 | tf_op jit(solution)/shard_map/cond/branch_1_fun/ppermute | solution.py:33
  160.2 1.2 maximum_maximum_fusion
  163.1 2.3 collective-permute-start.7
  165.3 4.5 %collective-permute-done.7 = bf16[64,1024]{1,0:T(8,128)(2,1)S(1)} collective-permute-done((bf16[64,1024]{1,0:T(8,128)(2,1)}, bf16[64,1024]{1,0:T(8,128)(2,1)S(1)}, u32[]{:S(2)}, u32[]{:S(2)}) %collective-permute-start.7) | collective-permute-done | bytes 131104 | tf_op jit(solution)/shard_map/cond/branch_1_fun/ppermute | solution.py:33
  169.9 4.9 %collective-permute-done.8 = bf16[64,1024]{1,0:T(8,128)(2,1)S(1)} collective-permute-done((bf16[64,1024]{1,0:T(8,128)(2,1)}, bf16[64,1024]{1,0:T(8,128)(2,1)S(1)}, u32[]{:S(2)}, u32[]{:S(2)}) %collective-permute-start.8) | collective-permute-done | bytes 131104 | tf_op jit(solution)/shard_map/cond/branch_1_fun/ppermute | solution.py:33
  174.8 1.7 convert_add_fusion.small_ref
  176.6 3.3 %inner_quarter.1 = (f32[80,1024]{1,0:T(8,128)}, bf16[3,80,1024]{2,1,0:T(8,128)(2,1)}) custom-call(s32[1]{0:T(128)} %bitcast.place_ref, bf16[256,1024]{1,0:T(8,128)(2,1)} %copy-done.16, bf16[256,1024]{1,0:T(8,128)(2,1)} %collective-permute-done.2.near_ref, bf16[256,1024]{1,0:T(8,128)(2,1)} %collective-permute-done.3.far_ref, ...), custom_call_target="tpu_custom_call" | custom-call | flops 1 | bytes 1 | tf_op jit(solution)/shard_map/cond/branch_1_fun/inner_quarter/pallas_call | solution.py:805
  179.9 1.1 slice_bitcast_fusion.2
  181.7 3.3 %collective-permute-start.11 = (bf16[80,1024]{1,0:T(8,128)(2,1)S(1)}, bf16[80,1024]{1,0:T(8,128)(2,1)S(1)}, u32[]{:S(2)}, u32[]{:S(2)}) collective-permute-start(bf16[80,1024]{1,0:T(8,128)(2,1)S(1)} %get-tuple-element.347), channel_id=1, source_target_pairs={{0,24},{2,26},{4,28},{6,30},{8,16},{10,18},{12,20},{14,22},{16,8},... | collective-permute-start | bytes 491528 | tf_op jit(solution)/shard_map/cond/branch_1_fun/ppermute | solution.py:33
  185.0 14.2 %collective-permute-done.10 = bf16[80,1024]{1,0:T(8,128)(2,1)S(1)} collective-permute-done((bf16[80,1024]{1,0:T(8,128)(2,1)S(1)}, bf16[80,1024]{1,0:T(8,128)(2,1)S(1)}, u32[]{:S(2)}, u32[]{:S(2)}) %collective-permute-start.10) | collective-permute-done | bytes 163872 | tf_op jit(solution)/shard_map/cond/branch_1_fun/ppermute | solution.py:33
  200.2 1.8 collective-permute-done.9
  203.0 4.8 %collective-permute-start.14 = (bf16[80,1024]{1,0:T(8,128)(2,1)S(1)}, bf16[80,1024]{1,0:T(8,128)(2,1)S(1)}, u32[]{:S(2)}, u32[]{:S(2)}) collective-permute-start(bf16[80,1024]{1,0:T(8,128)(2,1)S(1)} %add_convert_fusion), channel_id=1, source_target_pairs={{0,8},{2,10},{4,12},{6,14},{8,0},{10,2},{12,4},{14,6},{16,24},{18,... | collective-permute-start | bytes 491528 | tf_op jit(solution)/shard_map/cond/branch_1_fun/ppermute | solution.py:33
  207.7 2.3 fusion.41
  210.0 1.2 collective-permute-start.12
  211.5 6.9 %collective-permute-done.14 = bf16[80,1024]{1,0:T(8,128)(2,1)S(1)} collective-permute-done((bf16[80,1024]{1,0:T(8,128)(2,1)S(1)}, bf16[80,1024]{1,0:T(8,128)(2,1)S(1)}, u32[]{:S(2)}, u32[]{:S(2)}) %collective-permute-start.14) | collective-permute-done | bytes 163872 | tf_op jit(solution)/shard_map/cond/branch_1_fun/ppermute | solution.py:33
  219.1 8.7 %collective-permute-done.13 = bf16[80,1024]{1,0:T(8,128)(2,1)S(1)} collective-permute-done((bf16[80,1024]{1,0:T(8,128)(2,1)S(1)}, bf16[80,1024]{1,0:T(8,128)(2,1)S(1)}, u32[]{:S(2)}, u32[]{:S(2)}) %collective-permute-start.13) | collective-permute-done | bytes 163872 | tf_op jit(solution)/shard_map/cond/branch_1_fun/ppermute | solution.py:33
  229.7 1.3 slice_select_fusion
  232.0 1.1 broadcast_select_fusion.8
  235.3 9.9 %collective-permute-done.30.inner_ref = bf16[320,1024]{1,0:T(8,128)(2,1)S(1)} collective-permute-done((bf16[320,1024]{1,0:T(8,128)(2,1)}, bf16[320,1024]{1,0:T(8,128)(2,1)S(1)}, u32[]{:S(2)}, u32[]{:S(2)}) %collective-permute-start.30) | collective-permute-done | bytes 655392 | tf_op jit(solution)/shard_map/ppermute | solution.py:33
  245.4 10.6 %collective-permute-done.29 = f32[256,1]{0,1:T(1,128)S(1)} collective-permute-done((f32[256,1]{0,1:T(1,128)}, f32[256,1]{0,1:T(1,128)S(1)}, u32[]{:S(2)}, u32[]{:S(2)}) %collective-permute-start.29) | collective-permute-done | bytes 1056 | tf_op jit(solution)/shard_map/ppermute | solution.py:33
  256.7 2.1 fusion.29
  258.8 2.7 joined.4
  261.5 2.7 joined.5
  264.1 2.7 joined.6
  267.7 2.7 joined.7
  270.3 2.1 small_parts.1
  272.4 4.1 %convert_element_type.85 = f32[1024,1024]{1,0:T(8,128)} convert(bf16[1024,1024]{1,0:T(8,128)(2,1)} %get-tuple-element.329) | non-fusion elementwise | flops 1048576 | bytes 6291456 | tf_op jit(solution)/shard_map/convert_element_type | solution.py:1098
  (182 shorter events, 34.0 us)
Async XLA Ops:
  7.2 27.0 %copy-start = (bf16[1024,1024]{1,0:T(8,128)(2,1)S(1)}, bf16[1024,1024]{1,0:T(8,128)(2,1)}, u32[]{:S(2)}) copy-start(bf16[1024,1024]{1,0:T(8,128)(2,1)} %param.25) | copy-start | bytes 6291460
  7.2 251.6 %all-reduce.4.cloned.1.call-start = ((), (), s32[]{:S(2)}) async-start(), calls=%async_computation | async-start | bytes 8388608 | tf_op jit(solution)/shard_map/psum | solution.py:1002
  7.2 15.1 %collective-permute-start.15 = (bf16[256,512]{1,0:T(8,128)(2,1)}, bf16[256,512]{1,0:T(8,128)(2,1)S(1)}, u32[]{:S(2)}, u32[]{:S(2)}) collective-permute-start(bf16[256,512]{1,0:T(8,128)(2,1)} %own_ref.1), channel_id=1, source_target_pairs={{0,1},{1,0},{2,3},{3,2},{4,5},{5,4},{6,7},{7,6},{8,9},{9,8},{10,11... | collective-permute-start | bytes 786440 | tf_op jit(solution)/shard_map/ppermute | solution.py:33
  11.6 10.7 %collective-permute-start.16 = (bf16[16,512]{1,0:T(8,128)(2,1)}, bf16[16,512]{1,0:T(8,128)(2,1)S(1)}, u32[]{:S(2)}, u32[]{:S(2)}) collective-permute-start(bf16[16,512]{1,0:T(8,128)(2,1)} %edge_rows.1), channel_id=1, source_target_pairs={{0,2},{2,4},{4,6},{6,8},{8,10},{10,12},{12,14},{14,16},{16,18},{18... | collective-permute-start | bytes 49160 | tf_op jit(solution)/shard_map/ppermute | solution.py:28
  13.1 9.2 %collective-permute-start.17 = (bf16[16,512]{1,0:T(8,128)(2,1)}, bf16[16,512]{1,0:T(8,128)(2,1)S(1)}, u32[]{:S(2)}, u32[]{:S(2)}) collective-permute-start(bf16[16,512]{1,0:T(8,128)(2,1)} %edge_rows.1), channel_id=1, source_target_pairs={{0,3},{1,2},{2,5},{3,4},{4,7},{5,6},{6,9},{7,8},{8,11},{9,10},{10,... | collective-permute-start | bytes 49160 | tf_op jit(solution)/shard_map/ppermute | solution.py:51
  17.2 15.9 %collective-permute-start.19 = (bf16[256,512]{1,0:T(8,128)(2,1)}, bf16[256,512]{1,0:T(8,128)(2,1)}, u32[]{:S(2)}, u32[]{:S(2)}) collective-permute-start(bf16[256,512]{1,0:T(8,128)(2,1)} %param.27), channel_id=1, source_target_pairs={{0,1},{1,0},{2,3},{3,2},{4,5},{5,4},{6,7},{7,6},{8,9},{9,8},{10,11... | collective-permute-start | bytes 786440 | tf_op jit(solution)/shard_map/ppermute | solution.py:33
  25.3 7.8 %copy-start.18 = (bf16[256,512]{1,0:T(8,128)(2,1)S(1)}, bf16[256,512]{1,0:T(8,128)(2,1)}, u32[]{:S(2)}) copy-start(bf16[256,512]{1,0:T(8,128)(2,1)} %param.27) | copy-start | bytes 786436
  32.5 4.6 %collective-permute-start.18 = (f32[96,256]{1,0:T(8,128)S(1)}, f32[96,256]{1,0:T(8,128)S(1)}, u32[]{:S(2)}, u32[]{:S(2)}) collective-permute-start(f32[96,256]{1,0:T(8,128)S(1)} %get-tuple-element.130.selected_ref), channel_id=1, source_target_pairs={{0,1},{1,0},{2,3},{3,2},{4,5},{5,4},{6,7},{7,6},{8,9},{9,8},{10,11... | collective-permute-start | bytes 294920 | tf_op jit(solution)/shard_map/ppermute | solution.py:33
  34.1 13.4 %copy-start.13 = (bf16[256,512]{1,0:T(8,128)(2,1)}, bf16[256,512]{1,0:T(8,128)(2,1)S(1)}, u32[]{:S(2)}) copy-start(bf16[256,512]{1,0:T(8,128)(2,1)S(1)} %get-tuple-element.359) | copy-start | bytes 786436
  37.1 10.4 %copy-start.24 = (f32[96,256]{1,0:T(8,128)}, f32[96,256]{1,0:T(8,128)S(1)}, u32[]{:S(2)}) copy-start(f32[96,256]{1,0:T(8,128)S(1)} %collective-permute-done.18.other_ref) | copy-start | bytes 294916
  47.5 1.8 collective-permute-start.20
  52.4 6.6 %collective-permute-start.21 = (f32[40,1024]{1,0:T(8,128)}, f32[40,1024]{1,0:T(8,128)}, u32[]{:S(2)}, u32[]{:S(2)}) collective-permute-start(f32[40,1024]{1,0:T(8,128)} %pad_maximum_fusion.8), channel_id=1, source_target_pairs={{0,4},{2,6},{4,0},{6,2},{8,12},{10,14},{12,8},{14,10},{16,20},{18,... | collective-permute-start | bytes 491528 | tf_op jit(solution)/shard_map/ppermute | solution.py:33
  54.6 14.8 %copy-start.2 = (f32[256,1024]{1,0:T(8,128)S(1)}, f32[256,1024]{1,0:T(8,128)}, u32[]{:S(2)}) copy-start(f32[256,1024]{1,0:T(8,128)} %copy-done.1) | copy-start | bytes 3145732
  54.7 14.8 %copy-start.7 = (bf16[256,1024]{1,0:T(8,128)(2,1)S(1)}, bf16[256,1024]{1,0:T(8,128)(2,1)}, u32[]{:S(2)}) copy-start(bf16[256,1024]{1,0:T(8,128)(2,1)} %copy-done.6) | copy-start | bytes 1572868
  54.7 14.8 %copy-start.10 = (f32[256,1024]{1,0:T(8,128)S(1)}, f32[256,1024]{1,0:T(8,128)}, u32[]{:S(2)}) copy-start(f32[256,1024]{1,0:T(8,128)} %get-tuple-element.132.step_ref) | copy-start | bytes 3145732
  54.7 14.8 %copy-start.22 = (f32[96,256]{1,0:T(8,128)S(1)}, f32[96,256]{1,0:T(8,128)}, u32[]{:S(2)}) copy-start(f32[96,256]{1,0:T(8,128)} %copy-done.21) | copy-start | bytes 294916
  54.7 14.8 %copy-start.25 = (f32[96,256]{1,0:T(8,128)S(1)}, f32[96,256]{1,0:T(8,128)}, u32[]{:S(2)}) copy-start(f32[96,256]{1,0:T(8,128)} %copy-done.24) | copy-start | bytes 294916
  61.3 6.5 %collective-permute-start.22 = (f32[16,1024]{1,0:T(8,128)S(1)}, f32[16,1024]{1,0:T(8,128)S(1)}, u32[]{:S(2)}, u32[]{:S(2)}) collective-permute-start(f32[16,1024]{1,0:T(8,128)S(1)} %multiply_add_fusion.2), channel_id=1, source_target_pairs={{0,8},{2,10},{4,12},{6,14},{8,16},{10,18},{12,20},{14,22},{16,24},... | collective-permute-start | bytes 196616 | tf_op jit(solution)/shard_map/ppermute | solution.py:28
  65.6 21.2 %collective-permute-start.25 = (bf16[256,256]{1,0:T(8,128)(2,1)}, bf16[256,256]{1,0:T(8,128)(2,1)}, u32[]{:S(2)}, u32[]{:S(2)}) collective-permute-start(bf16[256,256]{1,0:T(8,128)(2,1)} %get-tuple-element.357), channel_id=1, source_target_pairs={{0,4},{2,6},{4,0},{6,2},{8,12},{10,14},{12,8},{14,10},{16,20},{18,... | collective-permute-start | bytes 393224 | tf_op jit(solution)/shard_map/ppermute | solution.py:33
  67.1 19.7 %collective-permute-start.26 = (bf16[256,256]{1,0:T(8,128)(2,1)}, bf16[256,256]{1,0:T(8,128)(2,1)}, u32[]{:S(2)}, u32[]{:S(2)}) collective-permute-start(bf16[256,256]{1,0:T(8,128)(2,1)} %get-tuple-element.356), channel_id=1, source_target_pairs={{0,2},{2,0},{4,6},{6,4},{8,10},{10,8},{12,14},{14,12},{16,18},{18,... | collective-permute-start | bytes 393224 | tf_op jit(solution)/shard_map/ppermute | solution.py:33
  67.1 19.7 %collective-permute-start.27 = (bf16[256,256]{1,0:T(8,128)(2,1)}, bf16[256,256]{1,0:T(8,128)(2,1)}, u32[]{:S(2)}, u32[]{:S(2)}) collective-permute-start(bf16[256,256]{1,0:T(8,128)(2,1)} %get-tuple-element.355), channel_id=1, source_target_pairs={{0,6},{2,4},{4,2},{6,0},{8,14},{10,12},{12,10},{14,8},{16,22},{18,... | collective-permute-start | bytes 393224 | tf_op jit(solution)/shard_map/ppermute | solution.py:33
  69.4 9.8 %copy-start.31 = (f32[16,1024]{1,0:T(8,128)}, f32[16,1024]{1,0:T(8,128)S(1)}, u32[]{:S(2)}) copy-start(f32[16,1024]{1,0:T(8,128)S(1)} %get-tuple-element.365.entry_ref) | copy-start | bytes 196612
  69.5 9.7 %copy-start.17 = (bf16[272,1024]{1,0:T(8,128)(2,1)S(1)}, bf16[272,1024]{1,0:T(8,128)(2,1)}, u32[]{:S(2)}) copy-start(bf16[272,1024]{1,0:T(8,128)(2,1)} %get-tuple-element.129) | copy-start | bytes 1671172
  88.7 10.6 %copy-start.23 = (f32[96,256]{1,0:T(8,128)S(1)}, f32[96,256]{1,0:T(8,128)}, u32[]{:S(2)}) copy-start(f32[96,256]{1,0:T(8,128)} %copy-done.21) | copy-start | bytes 294916
  88.7 10.6 %copy-start.26 = (f32[96,256]{1,0:T(8,128)S(1)}, f32[96,256]{1,0:T(8,128)}, u32[]{:S(2)}) copy-start(f32[96,256]{1,0:T(8,128)} %copy-done.24) | copy-start | bytes 294916
  88.7 10.6 %copy-start.32 = (f32[16,1024]{1,0:T(8,128)S(1)}, f32[16,1024]{1,0:T(8,128)}, u32[]{:S(2)}) copy-start(f32[16,1024]{1,0:T(8,128)} %copy-done.31) | copy-start | bytes 196612
  88.7 10.6 %copy-start.50 = (f32[1,1024]{1,0:T(1,128)S(1)}, f32[1,1024]{1,0:T(1,128)}, u32[]{:S(2)}) copy-start(f32[1,1024]{1,0:T(1,128)} %get-tuple-element.370) | copy-start | bytes 12292
  88.7 8.1 %collective-permute-start.24 = (f32[16,1024]{1,0:T(8,128)S(1)}, f32[16,1024]{1,0:T(8,128)}, u32[]{:S(2)}, u32[]{:S(2)}) collective-permute-start(f32[16,1024]{1,0:T(8,128)S(1)} %copy-done.45), channel_id=1, source_target_pairs={{8,0},{10,2},{12,4},{14,6},{16,8},{18,10},{20,12},{22,14},{24,16},... | collective-permute-start | bytes 196616 | tf_op jit(solution)/shard_map/ppermute | solution.py:28
  102.8 24.4 %copy-start.51 = (s32[256]{0:T(256)S(1)}, s32[256]{0:T(256)}, u32[]{:S(2)}) copy-start(s32[256]{0:T(256)} %get-tuple-element.185) | copy-start | bytes 3076 | tf_op jit(solution)/shard_map/cond
  102.8 29.4 %copy-start.8 = (bf16[256,1024]{1,0:T(8,128)(2,1)S(1)}, bf16[256,1024]{1,0:T(8,128)(2,1)}, u32[]{:S(2)}) copy-start(bf16[256,1024]{1,0:T(8,128)(2,1)} %get-tuple-element.59.act_ref) | copy-start | bytes 1572868 | tf_op jit(solution)/shard_map/cond
  102.8 29.4 %copy-start.20 = (f32[256,1024]{1,0:T(8,128)S(1)}, f32[256,1024]{1,0:T(8,128)}, u32[]{:S(2)}) copy-start(f32[256,1024]{1,0:T(8,128)} %get-tuple-element.74.convolved_ref) | copy-start | bytes 3145732 | tf_op jit(solution)/shard_map/cond
  102.8 29.4 %copy-start.28 = (bf16[96,1024]{1,0:T(8,128)(2,1)S(1)}, bf16[96,1024]{1,0:T(8,128)(2,1)}, u32[]{:S(2)}) copy-start(bf16[96,1024]{1,0:T(8,128)(2,1)} %get-tuple-element.72.select_ref) | copy-start | bytes 589828 | tf_op jit(solution)/shard_map/cond
  102.8 29.4 %copy-start.44 = (f32[4,1024]{1,0:T(4,128)S(1)}, f32[4,1024]{1,0:T(4,128)}, u32[]{:S(2)}) copy-start(f32[4,1024]{1,0:T(4,128)} %get-tuple-element.75.conv_weight_ref) | copy-start | bytes 49156 | tf_op jit(solution)/shard_map/cond
  126.7 4.9 %collective-permute-start = (f32[96,256]{1,0:T(8,128)}, f32[96,256]{1,0:T(8,128)S(1)}, u32[]{:S(2)}, u32[]{:S(2)}) collective-permute-start(f32[96,256]{1,0:T(8,128)} %get-tuple-element.71.select_grad_ref), channel_id=1, source_target_pairs={{0,1},{1,0},{2,3},{3,2},{4,5},{5,4},{6,7},{7,6},{8,9},{9,8},{10,11... | collective-permute-start | bytes 294920 | tf_op jit(solution)/shard_map/cond/branch_1_fun/ppermute | solution.py:33
  136.3 7.2 %copy-start.36 = (bf16[1,256,1024]{2,1,0:T(8,128)(2,1)S(1)}, bf16[1,256,1024]{2,1,0:T(8,128)(2,1)}, u32[]{:S(2)}) copy-start(bf16[1,256,1024]{2,1,0:T(8,128)(2,1)} %get-tuple-element.81) | copy-start | bytes 1572868 | tf_op jit(solution)/shard_map/cond
  136.3 7.2 %copy-start.47 = (f32[1024]{0:T(1024)S(1)}, f32[1024]{0:T(1024)}, u32[]{:S(2)}) copy-start(f32[1024]{0:T(1024)} %get-tuple-element.87) | copy-start | bytes 12292 | tf_op jit(solution)/shard_map/cond
  137.1 3.2 %collective-permute-start.1 = (f32[8,1024]{1,0:T(8,128)S(1)}, f32[8,1024]{1,0:T(8,128)S(1)}, u32[]{:S(2)}, u32[]{:S(2)}) collective-permute-start(f32[8,1024]{1,0:T(8,128)S(1)} %slice.72), channel_id=1, source_target_pairs={{2,0},{4,2},{6,4},{8,6},{10,8},{12,10},{14,12},{16,14},{18,16},{20... | collective-permute-start | bytes 98312 | tf_op jit(solution)/shard_map/cond/branch_1_fun/ppermute | solution.py:28
  141.2 8.7 %copy-start.16 = (bf16[256,1024]{1,0:T(8,128)(2,1)}, bf16[256,1024]{1,0:T(8,128)(2,1)S(1)}, u32[]{:S(2)}) copy-start(bf16[256,1024]{1,0:T(8,128)(2,1)S(1)} %get-tuple-element.345.own_ref) | copy-start | bytes 1572868 | tf_op jit(solution)/shard_map/cond
  141.3 18.1 %collective-permute-start.2 = (bf16[256,1024]{1,0:T(8,128)(2,1)S(1)}, bf16[256,1024]{1,0:T(8,128)(2,1)}, u32[]{:S(2)}, u32[]{:S(2)}) collective-permute-start(bf16[256,1024]{1,0:T(8,128)(2,1)S(1)} %get-tuple-element.345.own_ref), channel_id=1, source_target_pairs={{0,4},{2,6},{4,0},{6,2},{8,12},{10,14},{12,8},{14,10},{16,20},{18,... | collective-permute-start | bytes 1572872 | tf_op jit(solution)/shard_map/cond/branch_1_fun/ppermute | solution.py:33
  143.5 16.7 %copy-start.40 = (f32[96,1024]{1,0:T(8,128)S(1)}, f32[96,1024]{1,0:T(8,128)}, u32[]{:S(2)}) copy-start(f32[96,1024]{1,0:T(8,128)} %get-tuple-element.79) | copy-start | bytes 1179652 | tf_op jit(solution)/shard_map/cond
  149.3 27.2 %copy-start.9 = (bf16[4,256,256]{2,1,0:T(8,128)(2,1)S(1)}, bf16[4,256,256]{2,1,0:T(8,128)(2,1)}, u32[]{:S(2)}) copy-start(bf16[4,256,256]{2,1,0:T(8,128)(2,1)} %get-tuple-element.68.rest_0_.normed_ref) | copy-start | bytes 1572868 | tf_op jit(solution)/shard_map/cond
  149.3 3.6 %collective-permute-start.5 = (f32[1,1024]{1,0:T(1,128)S(1)}, f32[1,1024]{1,0:T(1,128)S(1)}, u32[]{:S(2)}, u32[]{:S(2)}) collective-permute-start(f32[1,1024]{1,0:T(1,128)S(1)} %bitcast.72), channel_id=1, source_target_pairs={{0,1},{1,0},{2,3},{3,2},{4,5},{5,4},{6,7},{7,6},{8,9},{9,8},{10,11... | collective-permute-start | bytes 12296 | tf_op jit(solution)/shard_map/cond/branch_1_fun/ppermute | solution.py:33
  149.9 26.6 %collective-permute-start.3 = (bf16[256,1024]{1,0:T(8,128)(2,1)S(1)}, bf16[256,1024]{1,0:T(8,128)(2,1)}, u32[]{:S(2)}, u32[]{:S(2)}) collective-permute-start(bf16[256,1024]{1,0:T(8,128)(2,1)S(1)} %get-tuple-element.345.own_ref), channel_id=1, source_target_pairs={{0,2},{2,0},{4,6},{6,4},{8,10},{10,8},{12,14},{14,12},{16,18},{18,... | collective-permute-start | bytes 1572872 | tf_op jit(solution)/shard_map/cond/branch_1_fun/ppermute | solution.py:33
  159.3 17.2 %collective-permute-start.4 = (bf16[256,1024]{1,0:T(8,128)(2,1)}, bf16[256,1024]{1,0:T(8,128)(2,1)}, u32[]{:S(2)}, u32[]{:S(2)}) collective-permute-start(bf16[256,1024]{1,0:T(8,128)(2,1)} %collective-permute-done.2.near_ref), channel_id=1, source_target_pairs={{0,2},{2,0},{4,6},{6,4},{8,10},{10,8},{12,14},{14,12},{16,18},{18,... | collective-permute-start | bytes 1572872 | tf_op jit(solution)/shard_map/cond/branch_1_fun/ppermute | solution.py:33
  163.1 2.3 collective-permute-start.6
  163.1 6.8 %collective-permute-start.7 = (bf16[64,1024]{1,0:T(8,128)(2,1)}, bf16[64,1024]{1,0:T(8,128)(2,1)S(1)}, u32[]{:S(2)}, u32[]{:S(2)}) collective-permute-start(bf16[64,1024]{1,0:T(8,128)(2,1)} %get-tuple-element.341), channel_id=1, source_target_pairs={{0,4},{2,6},{4,0},{6,2},{8,12},{10,14},{12,8},{14,10},{16,20},{18,... | collective-permute-start | bytes 393224 | tf_op jit(solution)/shard_map/cond/branch_1_fun/ppermute | solution.py:33
  165.3 9.5 %collective-permute-start.8 = (bf16[64,1024]{1,0:T(8,128)(2,1)}, bf16[64,1024]{1,0:T(8,128)(2,1)S(1)}, u32[]{:S(2)}, u32[]{:S(2)}) collective-permute-start(bf16[64,1024]{1,0:T(8,128)(2,1)} %get-tuple-element.340), channel_id=1, source_target_pairs={{0,6},{2,4},{4,2},{6,0},{8,14},{10,12},{12,10},{14,8},{16,22},{18,... | collective-permute-start | bytes 393224 | tf_op jit(solution)/shard_map/cond/branch_1_fun/ppermute | solution.py:33
  181.0 18.2 %collective-permute-start.10 = (bf16[80,1024]{1,0:T(8,128)(2,1)S(1)}, bf16[80,1024]{1,0:T(8,128)(2,1)S(1)}, u32[]{:S(2)}, u32[]{:S(2)}) collective-permute-start(bf16[80,1024]{1,0:T(8,128)(2,1)S(1)} %get-tuple-element.348), channel_id=1, source_target_pairs={{0,16},{2,18},{4,20},{6,22},{8,24},{10,26},{12,28},{14,30},{16,0},... | collective-permute-start | bytes 491528 | tf_op jit(solution)/shard_map/cond/branch_1_fun/ppermute | solution.py:33
  181.7 18.4 %collective-permute-start.11 = (bf16[80,1024]{1,0:T(8,128)(2,1)S(1)}, bf16[80,1024]{1,0:T(8,128)(2,1)S(1)}, u32[]{:S(2)}, u32[]{:S(2)}) collective-permute-start(bf16[80,1024]{1,0:T(8,128)(2,1)S(1)} %get-tuple-element.347), channel_id=1, source_target_pairs={{0,24},{2,26},{4,28},{6,30},{8,16},{10,18},{12,20},{14,22},{16,8},... | collective-permute-start | bytes 491528 | tf_op jit(solution)/shard_map/cond/branch_1_fun/ppermute | solution.py:33
  185.0 16.9 %collective-permute-start.9 = (bf16[80,1024]{1,0:T(8,128)(2,1)S(1)}, bf16[80,1024]{1,0:T(8,128)(2,1)S(1)}, u32[]{:S(2)}, u32[]{:S(2)}) collective-permute-start(bf16[80,1024]{1,0:T(8,128)(2,1)S(1)} %get-tuple-element.346), channel_id=1, source_target_pairs={{0,8},{2,10},{4,12},{6,14},{8,0},{10,2},{12,4},{14,6},{16,24},{18,... | collective-permute-start | bytes 491528 | tf_op jit(solution)/shard_map/cond/branch_1_fun/ppermute | solution.py:33
  203.0 15.5 %collective-permute-start.14 = (bf16[80,1024]{1,0:T(8,128)(2,1)S(1)}, bf16[80,1024]{1,0:T(8,128)(2,1)S(1)}, u32[]{:S(2)}, u32[]{:S(2)}) collective-permute-start(bf16[80,1024]{1,0:T(8,128)(2,1)S(1)} %add_convert_fusion), channel_id=1, source_target_pairs={{0,8},{2,10},{4,12},{6,14},{8,0},{10,2},{12,4},{14,6},{16,24},{18,... | collective-permute-start | bytes 491528 | tf_op jit(solution)/shard_map/cond/branch_1_fun/ppermute | solution.py:33
  210.0 9.1 %collective-permute-start.12 = (bf16[80,1024]{1,0:T(8,128)(2,1)S(1)}, bf16[80,1024]{1,0:T(8,128)(2,1)S(1)}, u32[]{:S(2)}, u32[]{:S(2)}) collective-permute-start(bf16[80,1024]{1,0:T(8,128)(2,1)S(1)} %add_convert_fusion), channel_id=1, source_target_pairs={{0,24},{2,26},{4,28},{6,30},{8,16},{10,18},{12,20},{14,22},{16,8},... | collective-permute-start | bytes 491528 | tf_op jit(solution)/shard_map/cond/branch_1_fun/ppermute | solution.py:33
  211.2 16.6 %collective-permute-start.13 = (bf16[80,1024]{1,0:T(8,128)(2,1)S(1)}, bf16[80,1024]{1,0:T(8,128)(2,1)S(1)}, u32[]{:S(2)}, u32[]{:S(2)}) collective-permute-start(bf16[80,1024]{1,0:T(8,128)(2,1)S(1)} %add_convert_fusion), channel_id=1, source_target_pairs={{0,16},{2,18},{4,20},{6,22},{8,24},{10,26},{12,28},{14,30},{16,0},... | collective-permute-start | bytes 491528 | tf_op jit(solution)/shard_map/cond/branch_1_fun/ppermute | solution.py:33
  228.9 16.3 %copy-start.37 = (f32[256,1]{1,0:T(8,128)S(1)}, f32[256,1]{1,0:T(8,128)}, u32[]{:S(2)}) copy-start(f32[256,1]{1,0:T(8,128)} %get-tuple-element.134) | copy-start | bytes 3076
  228.9 27.8 %copy-start.3 = (f32[256,1024]{1,0:T(8,128)S(1)}, f32[256,1024]{1,0:T(8,128)}, u32[]{:S(2)}) copy-start(f32[256,1024]{1,0:T(8,128)} %fusion.31) | copy-start | bytes 3145732
  228.9 27.8 %copy-start.15 = (bf16[256,512]{1,0:T(8,128)(2,1)S(1)}, bf16[256,512]{1,0:T(8,128)(2,1)}, u32[]{:S(2)}) copy-start(bf16[256,512]{1,0:T(8,128)(2,1)} %own_ref.1) | copy-start | bytes 786436
  228.9 27.8 %copy-start.19 = (bf16[256,512]{1,0:T(8,128)(2,1)S(1)}, bf16[256,512]{1,0:T(8,128)(2,1)}, u32[]{:S(2)}) copy-start(bf16[256,512]{1,0:T(8,128)(2,1)} %param.27) | copy-start | bytes 786436
  228.9 16.3 %collective-permute-start.30 = (bf16[320,1024]{1,0:T(8,128)(2,1)}, bf16[320,1024]{1,0:T(8,128)(2,1)S(1)}, u32[]{:S(2)}, u32[]{:S(2)}) collective-permute-start(bf16[320,1024]{1,0:T(8,128)(2,1)} %get-tuple-element.141.inner_ref), channel_id=1, source_target_pairs={{0,4},{2,6},{4,0},{6,2},{8,12},{10,14},{12,8},{14,10},{16,20},{18,... | collective-permute-start | bytes 1966088 | tf_op jit(solution)/shard_map/ppermute | solution.py:33
  230.9 25.7 %collective-permute-start.23 = (f32[256,512]{1,0:T(8,128)S(1)}, f32[256,512]{1,0:T(8,128)S(1)}, u32[]{:S(2)}, u32[]{:S(2)}) collective-permute-start(f32[256,512]{1,0:T(8,128)S(1)} %slice_select_fusion), channel_id=1, source_target_pairs={{0,1},{1,0},{2,3},{3,2},{4,5},{5,4},{6,7},{7,6},{8,9},{9,8},{10,11... | collective-permute-start | bytes 1572872 | tf_op jit(solution)/shard_map/ppermute | solution.py:33
  233.1 23.5 %collective-permute-start.28 = (f32[256,512]{1,0:T(8,128)S(1)}, f32[256,512]{1,0:T(8,128)S(1)}, u32[]{:S(2)}, u32[]{:S(2)}) collective-permute-start(f32[256,512]{1,0:T(8,128)S(1)} %broadcast_select_fusion.8), channel_id=1, source_target_pairs={{0,1},{1,0},{2,3},{3,2},{4,5},{5,4},{6,7},{7,6},{8,9},{9,8},{10,11... | collective-permute-start | bytes 1572872 | tf_op jit(solution)/shard_map/ppermute | solution.py:33
  234.2 27.2 %collective-permute-start.32 = (bf16[320,1024]{1,0:T(8,128)(2,1)}, bf16[320,1024]{1,0:T(8,128)(2,1)}, u32[]{:S(2)}, u32[]{:S(2)}) collective-permute-start(bf16[320,1024]{1,0:T(8,128)(2,1)} %get-tuple-element.141.inner_ref), channel_id=1, source_target_pairs={{0,2},{2,0},{4,6},{6,4},{8,10},{10,8},{12,14},{14,12},{16,18},{18,... | collective-permute-start | bytes 1966088 | tf_op jit(solution)/shard_map/ppermute | solution.py:33
  234.2 21.7 %collective-permute-start.29 = (f32[256,1]{0,1:T(1,128)}, f32[256,1]{0,1:T(1,128)S(1)}, u32[]{:S(2)}, u32[]{:S(2)}) collective-permute-start(f32[256,1]{0,1:T(1,128)} %get-tuple-element.140), channel_id=1, source_target_pairs={{0,1},{1,0},{2,3},{3,2},{4,5},{5,4},{6,7},{7,6},{8,9},{9,8},{10,11... | collective-permute-start | bytes 3080 | tf_op jit(solution)/shard_map/ppermute | solution.py:33
  245.2 13.6 %copy-start.29 = (bf16[320,1024]{1,0:T(8,128)(2,1)}, bf16[320,1024]{1,0:T(8,128)(2,1)S(1)}, u32[]{:S(2)}) copy-start(bf16[320,1024]{1,0:T(8,128)(2,1)S(1)} %collective-permute-done.30.inner_ref) | copy-start | bytes 1966084
  245.2 21.6 %collective-permute-start.31 = (bf16[320,1024]{1,0:T(8,128)(2,1)S(1)}, bf16[320,1024]{1,0:T(8,128)(2,1)S(1)}, u32[]{:S(2)}, u32[]{:S(2)}) collective-permute-start(bf16[320,1024]{1,0:T(8,128)(2,1)S(1)} %collective-permute-done.30.inner_ref), channel_id=1, source_target_pairs={{0,2},{2,0},{4,6},{6,4},{8,10},{10,8},{12,14},{14,12},{16,18},{18,... | collective-permute-start | bytes 1966088 | tf_op jit(solution)/shard_map/ppermute | solution.py:33
  (22 other events, 62.7 us)
Sparse Core Ops, SparseCore 0:
  84.7 135.6 all-reduce.3

commit v8 on v7

--- a/solution.py
+++ b/solution.py
@@ -355,9 +355,11 @@
     gated_grad_ref,
     mask_ref,
     decay_log_ref,
-    entry_ref,
+    passed_ref,
+    entering_ref,
     skip_ref,
     pair_ref,
+    entry_ref,
     coef,
     held_step,
     drive,
@@ -367,7 +369,11 @@
     rows = step_ref.shape[0]
     count = decay_log_ref.shape[0]
     rank = selected_ref.shape[0] - 2 * count
-    decay2 = -jnp.exp(decay_log_ref[...]) * log2e
+    decay = -jnp.exp(decay_log_ref[...])
+    decay2 = decay * log2e
+    before_steps = passed_ref[2 * count : 2 * count + 1, :]
+    entry = passed_ref[:count, :] + through(decay, before_steps) * entering_ref[...]
+    entry_ref[...] = entry
     coef[...] = selected_ref[rank:, :] + other_ref[rank:, :]
     act = act_ref[...].astype(f32)
     held_step[...] = jnp.where(mask_ref[:, 1:2] > 0.0, step_ref[...], reset_step)
@@ -383,7 +389,7 @@
         put_state_sums(halves, scanned, block)
         return state
 
-    lax.fori_loop(0, rows // body_rows, forward, entry_ref[...])
+    lax.fori_loop(0, rows // body_rows, forward, entry)
     gate = gate_ref[...].astype(f32)
     logistic = jax.nn.sigmoid(gate)
     total = scanned[...] + skip_ref[...] * act
@@ -393,7 +399,7 @@
 
 
 def scan_forward(
-    selected, other, step, act, projected, gated_grad, masks, decay_log, entry, skip_gain
+    selected, other, step, act, projected, gated_grad, masks, decay_log, passed, entering, skip_gain
 ):
     rows, width = step.shape
     count = decay_log.shape[0]
@@ -411,11 +417,15 @@
             column_spec(rows),
             whole_spec(rows, masks.shape[1]),
             column_spec(count),
+            column_spec(2 * count + 8),
             column_spec(count),
             column_spec(1),
         ],
-        pl.BlockSpec((2, rows, scan_width), lambda j: (0, 0, j)),
-        jax.ShapeDtypeStruct((2, rows, width), bf16),
+        [pl.BlockSpec((2, rows, scan_width), lambda j: (0, 0, j)), column_spec(count)],
+        [
+            jax.ShapeDtypeStruct((2, rows, width), bf16),
+            jax.ShapeDtypeStruct((count, width), f32),
+        ],
         [pltpu.VMEM((2 * count, rows), f32)]
         + [pltpu.VMEM((rows, scan_width), f32)] * 3
         + [pltpu.VMEM((8 * body_rows * (scan_width // lanes), lanes), f32)],
@@ -427,7 +437,8 @@
         gated_grad,
         masks,
         decay_log,
-        entry,
+        passed,
+        entering,
         skip_gain,
     )
 
@@ -443,35 +454,34 @@
     mask_ref,
     decay_log_ref,
     entry_ref,
-    tail_ref,
+    passed_ref,
+    returning_ref,
     skip_ref,
     step_weight_ref,
-    *rest,
-    waits,
+    act_grad_ref,
+    select_grad_ref,
+    small_ref,
+    coef,
+    held_step,
+    drive,
+    scan_grad,
+    weighted,
+    held_sum,
+    states,
+    factors,
+    halves,
+    more_halves,
+    in_sum,
+    read_sum,
 ):
-    (
-        act_grad_ref,
-        select_grad_ref,
-        small_ref,
-        coef,
-        held_step,
-        drive,
-        scan_grad,
-        weighted,
-        held_sum,
-        states,
-        factors,
-        halves,
-        more_halves,
-        in_sum,
-        read_sum,
-    ) = rest[waits:]
     rows = step_ref.shape[0]
     count = decay_log_ref.shape[0]
     rank = step_weight_ref.shape[0]
     blocks = rows // body_rows
     decay = -jnp.exp(decay_log_ref[...])
     decay2 = decay * log2e
+    after_steps = passed_ref[2 * count + 1 : 2 * count + 2, :]
+    tail = passed_ref[count : 2 * count, :] + through(decay, after_steps) * returning_ref[...]
     selected = selected_ref[...] + other_ref[...]
     coef[...] = selected[rank:, :]
     step_low = selected[:rank, :].astype(bf16)
@@ -526,7 +536,7 @@
         return adjoint, decay_grad
 
     ignored, decay_grad = lax.fori_loop(
-        0, blocks, backward, (tail_ref[...], jnp.zeros(decay.shape, f32))
+        0, blocks, backward, (tail, jnp.zeros(decay.shape, f32))
     )
     act_grad_ref[...] = step * weighted[...] + skip_ref[...] * scan_grad[...]
     step_grad = act * weighted[...] + held_sum[...]
@@ -560,10 +570,10 @@
     masks,
     decay_log,
     entry,
-    tail,
+    passed,
+    returning,
     skip_gain,
     step_weight,
-    waits,
 ):
     rows, width = step.shape
     count = decay_log.shape[0]
@@ -572,7 +582,7 @@
     half_rows = 8 * body_rows * (scan_width // lanes)
     small = rank + count + 16
     return call(
-        functools.partial(backward_kernel, waits=len(waits)),
+        backward_kernel,
         "scan_backward",
         width,
         [
@@ -586,11 +596,11 @@
             whole_spec(rows, masks.shape[1]),
             column_spec(count),
             column_spec(count),
+            column_spec(2 * count + 8),
             column_spec(count),
             column_spec(1),
             column_spec(rank),
-        ]
-        + [pl.BlockSpec(memory_space=pl.ANY)] * len(waits),
+        ],
         [column_spec(rows), whole_spec(columns, rows), column_spec(small)],
         [
             jax.ShapeDtypeStruct((rows, width), f32),
@@ -617,10 +627,10 @@
         masks,
         decay_log,
         entry,
-        tail,
+        passed,
+        returning,
         skip_gain,
         step_weight,
-        *waits,
     )
 
 
@@ -634,6 +644,7 @@
     inner_ref,
     conv_weight_ref,
     mask_ref,
+    wait_ref,
     inner_grad_ref,
     edge_ref,
     small_ref,
@@ -678,7 +689,7 @@
 
 
 def convolve_grad(
-    select_grad, other, select_weight, act_grad, convolved, act, projected, conv_weight, masks
+    select_grad, other, select_weight, act_grad, convolved, act, projected, conv_weight, masks, wait
 ):
     rows, width = act.shape
     extended = rows + halo
@@ -699,6 +710,7 @@
             part_spec(0, extended),
             column_spec(taps),
             whole_spec(rows, masks.shape[1]),
+            pl.BlockSpec(memory_space=pl.ANY),
         ],
         [column_spec(rows), column_spec(16), column_spec(small)],
         [
@@ -716,13 +728,31 @@
         projected,
         conv_weight,
         masks,
+        wait,
     )
 
 
 def normalize_kernel(
-    own_ref, other_ref, edge_ref, other_edge_ref, gain_ref, whole_ref, normed_ref, inverse_ref
+    own_ref,
+    other_ref,
+    edge_ref,
+    other_edge_ref,
+    gain_ref,
+    ids_ref,
+    whole_ref,
+    normed_ref,
+    inverse_ref,
+    mask_ref,
 ):
     rows, half = own_ref.shape
+    ids = ids_ref[...].astype(f32)
+    place = lax.broadcasted_iota(jnp.int32, ids.shape, 1)
+    same = []
+    for lag in range(8):
+        earlier = jnp.where(place < lag, ids[:, :1], pltpu.roll(ids, lag, 1)) if lag else ids
+        same.append(jnp.where(earlier == ids, 1.0, 0.0))
+    spare = jnp.zeros((lanes - 8, rows), f32)
+    mask_ref[...] = jnp.concatenate(same + [spare]).T
     right = lax.axis_index("narrow") == 1
     for at, own, other in ((0, own_ref, other_ref), (rows, edge_ref, other_edge_ref)):
         end = at + own.shape[0]
@@ -734,7 +764,7 @@
     inverse_ref[...] = inverse[:rows]
 
 
-def normalized(own, other, edge, other_edge, gain):
+def normalized(own, other, edge, other_edge, gain, ids):
     rows, half = own.shape
     extended = rows + edge.shape[0]
     return pl.pallas_call(
@@ -743,10 +773,24 @@
             jax.ShapeDtypeStruct((extended, 2 * half), bf16),
             jax.ShapeDtypeStruct((extended, 2 * half), bf16),
             jax.ShapeDtypeStruct((rows, 1), f32),
+            jax.ShapeDtypeStruct((rows, lanes), f32),
         ],
         cost_estimate=tiny_cost,
         name="normalized",
-    )(own, other, edge, other_edge, gain)
+    )(own, other, edge, other_edge, gain, ids)
+
+
+def after(array, *waits):
+    anywhere = pl.BlockSpec(memory_space=pl.ANY)
+    return pl.pallas_call(
+        lambda *refs: None,
+        in_specs=[anywhere] * (1 + len(waits)),
+        out_specs=anywhere,
+        out_shape=jax.ShapeDtypeStruct(array.shape, array.dtype),
+        input_output_aliases={0: 0},
+        cost_estimate=tiny_cost,
+        name="after",
+    )(array, *waits)
 
 
 def edge_kernel(ids_ref, tokens_ref, out_ref):
@@ -777,44 +821,95 @@
     )(ids, tokens)
 
 
+def small_kernel(place_ref, scan_ref, conv_ref, gain_ref, other_gain_ref, keep_ref, sends_ref, rows):
+    at = 0
+    for ref in (scan_ref, conv_ref):
+        rows[at : at + ref.shape[0], :] = ref[...]
+        at += ref.shape[0]
+    rows[at:, :] = jnp.broadcast_to(
+        gain_ref[...] + other_gain_ref[...], (rows.shape[0] - at, rows.shape[1])
+    )
+    quarter = keep_ref.shape[0]
+    for n in range(4):
+        start = pl.multiple_of((place_ref[0] ^ n) * quarter, quarter)
+        block = rows[pl.ds(start, quarter), :]
+        if n == 0:
+            keep_ref[...] = block
+        else:
+            sends_ref[n - 1] = block.astype(bf16)
+
+
+def small_quarters(place, scan_small, conv_small, gain, other_gain):
+    width = scan_small.shape[1]
+    rows = -(-(scan_small.shape[0] + conv_small.shape[0] + 1) // 256) * 256
+    return pl.pallas_call(
+        small_kernel,
+        in_specs=[pl.BlockSpec(memory_space=pltpu.SMEM)]
+        + [pl.BlockSpec(memory_space=pltpu.VMEM)] * 4,
+        out_shape=[
+            jax.ShapeDtypeStruct((rows // 4, width), f32),
+            jax.ShapeDtypeStruct((3, rows // 4, width), bf16),
+        ],
+        scratch_shapes=[pltpu.VMEM((rows, width), f32)],
+        cost_estimate=tiny_cost,
+        name="small_quarters",
+    )(place, scan_small, conv_small, gain, other_gain)
+
+
 def quarter_kernel(
-    place_ref, own_ref, near_ref, far_ref, last_ref, normed_ref, small_ref, keep_ref, send_refs, piece
+    place_ref,
+    own_ref,
+    near_ref,
+    far_ref,
+    last_ref,
+    normed_ref,
+    small_ref,
+    first_ref,
+    second_ref,
+    third_ref,
+    *rest,
 ):
+    keep_ref, sends_ref, piece, small = rest[-4:]
     total = None
     for n, grads in enumerate((own_ref, near_ref, far_ref, last_ref)):
         part = lax.dot_general(normed_ref[n], grads[...], contract_first, preferred_element_type=f32)
         total = part if total is None else total + part
     piece[...] = total
+    small[...] = small_ref[...] + sum(
+        ref[...].astype(f32) for ref in (first_ref, second_ref, third_ref)
+    )
+    rows, spare = piece.shape[0] // 4, small.shape[0] // 4
     for n in range(4):
         block = place_ref[0] ^ n
-        rows, spare = piece.shape[0] // 4, small_ref.shape[0] // 4
-        inner = piece[pl.ds(pl.multiple_of(block * rows, rows), rows), :]
-        small = small_ref[pl.ds(pl.multiple_of(block * spare, spare), spare), :]
+        inner_rows = piece[pl.ds(pl.multiple_of(block * rows, rows), rows), :]
+        small_rows = small[pl.ds(pl.multiple_of(block * spare, spare), spare), :]
         if n == 0:
-            keep_ref[:rows, :] = inner
-            keep_ref[rows:, :] = small
+            keep_ref[:rows, :] = inner_rows
+            keep_ref[rows:, :] = small_rows
         else:
-            send_refs[n - 1, :rows, :] = inner.astype(bf16)
-            send_refs[n - 1, rows:, :] = small.astype(bf16)
-
-
-def inner_quarter(place, own, near, far, last, normed, small):
+            sends_ref[n - 1, :rows, :] = inner_rows.astype(bf16)
+            sends_ref[n - 1, rows:, :] = small_rows.astype(bf16)
+
+
+def inner_quarter(place, own, near, far, last, normed, smalls, waits):
     width = own.shape[1]
     quarter = normed.shape[2]
-    rows = (quarter + small.shape[0]) // 4
+    spare = smalls[0].shape[0]
+    rows = (quarter + spare) // 4
     return pl.pallas_call(
         quarter_kernel,
         in_specs=[pl.BlockSpec(memory_space=pltpu.SMEM)]
-        + [pl.BlockSpec(memory_space=pltpu.VMEM)] * 6,
+        + [pl.BlockSpec(memory_space=pltpu.VMEM)] * 9
+        + [pl.BlockSpec(memory_space=pl.ANY)] * len(waits),
         out_shape=[
             jax.ShapeDtypeStruct((rows, width), f32),
             jax.ShapeDtypeStruct((3, rows, width), bf16),
         ],
-        scratch_shapes=[pltpu.VMEM((quarter, width), f32)],
+        scratch_shapes=[pltpu.VMEM((quarter, width), f32), pltpu.VMEM((spare, width), f32)],
         compiler_params=pltpu.CompilerParams(vmem_limit_bytes=vmem_bytes),
         cost_estimate=tiny_cost,
         name="inner_quarter",
-    )(place, own, near, far, last, normed, small)
+    )(place, own, near, far, last, normed, *smalls, *waits)
 
 
 def join_kernel(place_ref, gate_ref, inner_ref, *rest):
@@ -876,41 +971,55 @@
     )(small)
 
 
-def carried(ends, decay):
-    count = decay.shape[0]
-    place = lax.axis_index("wide")
-
-    def split(packed):
-        return packed[:count], packed[count : 2 * count], packed[2 * count : 2 * count + 1]
-
-    def through(total):
-        return jnp.exp(decay * total)
-
-    zero = jnp.zeros(decay.shape, f32)
-    none = jnp.zeros((1, decay.shape[1]), f32)
-    before, before_steps, after, after_steps = zero, none, zero, none
+def through(decay, total):
+    return jnp.exp(decay * total)
+
+
+def round_kernel(second_ref, decay_log_ref, own_ref, other_ref, passed_ref, ends_ref, new_passed_ref):
+    count = decay_log_ref.shape[0]
+    decay = -jnp.exp(decay_log_ref[...])
+    second = second_ref[0] > 0
+
+    def split(ref):
+        return ref[:count], ref[count : 2 * count], ref[2 * count : 2 * count + 1]
+
+    own, other = split(own_ref), split(other_ref)
+    early = [jnp.where(second, b, a) for a, b in zip(own, other)]
+    late = [jnp.where(second, a, b) for a, b in zip(own, other)]
+    ends_ref[:count, :] = late[0] + through(decay, late[2]) * early[0]
+    ends_ref[count : 2 * count, :] = early[1] + through(decay, early[2]) * late[1]
+    ends_ref[2 * count :, :] = jnp.broadcast_to(early[2] + late[2], (8, decay.shape[1]))
+    before, after = passed_ref[:count], passed_ref[count : 2 * count]
+    before_steps = passed_ref[2 * count : 2 * count + 1]
+    after_steps = passed_ref[2 * count + 1 : 2 * count + 2]
+    new_passed_ref[:count, :] = before + jnp.where(second, through(decay, before_steps) * other[0], 0.0)
+    new_passed_ref[count : 2 * count, :] = after + jnp.where(
+        second, 0.0, through(decay, after_steps) * other[1]
+    )
+    new_passed_ref[2 * count : 2 * count + 1, :] = before_steps + jnp.where(second, other[2], 0.0)
+    new_passed_ref[2 * count + 1 : 2 * count + 2, :] = after_steps + jnp.where(second, 0.0, other[2])
+
+
+def carried(ends, decay_log):
+    count, width = decay_log.shape
+    place = lax.axis_index("wide").astype(jnp.int32)
+    passed = jnp.zeros((2 * count + 8, width), f32)
     packed = ends
-    for bit in (1, 2):
-        second = (place & bit) != 0
-        own = split(packed)
-        other = split(swapped(packed, "wide", bit))
-        early = [jnp.where(second, b, a) for a, b in zip(own, other)]
-        late = [jnp.where(second, a, b) for a, b in zip(own, other)]
-        before = before + jnp.where(second, through(before_steps) * other[0], 0.0)
-        before_steps = before_steps + jnp.where(second, other[2], 0.0)
-        after = after + jnp.where(second, 0.0, through(after_steps) * other[1])
-        after_steps = after_steps + jnp.where(second, 0.0, other[2])
-        state = late[0] + through(late[2]) * early[0]
-        adjoint = early[1] + through(early[2]) * late[1]
-        packed = jnp.concatenate(
-            [state, adjoint, jnp.broadcast_to(early[2] + late[2], (8, decay.shape[1]))]
-        )
+    vmem = pl.BlockSpec(memory_space=pltpu.VMEM)
+    for k in range(2):
+        packed, passed = pl.pallas_call(
+            round_kernel,
+            in_specs=[pl.BlockSpec(memory_space=pltpu.SMEM)] + [vmem] * 4,
+            out_shape=[
+                jax.ShapeDtypeStruct(ends.shape, f32),
+                jax.ShapeDtypeStruct(passed.shape, f32),
+            ],
+            cost_estimate=tiny_cost,
+            name="carry_round",
+        )((place >> k & 1)[None], decay_log, packed, swapped(packed, "wide", 2**k), passed)
     from_before = passed_along(packed[:count], "wide", 4)
     from_after = passed_along(packed[count : 2 * count], "wide", -4)
-    return (
-        before + through(before_steps) * from_before,
-        after + through(after_steps) * from_after,
-    )
+    return passed, from_before, from_after
 
 
 def local(
@@ -945,17 +1054,8 @@
     edge, other_edge = to_next_both(edge_rows_of(segment_ids, tokens))
 
     same_as_last = (segment_ids[rows - 8 :] == segment_ids[rows - 1 :])[:, None]
-    padded_ids = jnp.concatenate([jnp.broadcast_to(segment_ids[:1], (taps - 1,)), segment_ids])
-    masks = jnp.stack(
-        [
-            (padded_ids[taps - 1 - lag : taps - 1 - lag + rows] == segment_ids).astype(f32)
-            for lag in range(taps)
-        ]
-        + [jnp.zeros((rows,), f32)] * (8 - taps),
-        axis=1,
-    )
-    whole_ext, normed_ext, inverse = normalized(
-        tokens, other_tokens, edge, other_edge, norm_gain[None]
+    whole_ext, normed_ext, inverse, masks = normalized(
+        tokens, other_tokens, edge, other_edge, norm_gain[None], segment_ids[None]
     )
     projected = jnp.einsum(
         "td,dce->cte", normed_ext, in_weight, preferred_element_type=f32
@@ -979,8 +1079,8 @@
         masks,
         decay_log,
     )
-    entry, tail = carried(ends, -jnp.exp(decay_log))
-    pair = scan_forward(
+    passed, entering, returning = carried(ends, decay_log)
+    pair, entry = scan_forward(
         selected,
         other_selected,
         step,
@@ -989,12 +1089,13 @@
         gated_grad,
         masks,
         decay_log,
-        entry,
+        passed,
+        entering,
         skip_gain[None],
     )
     gated, gate_grad = pair[0], pair[1]
     normed = normed_ext[:rows]
-    normed_four = quarter_of_four(normed)
+    normed_four = quarter_of_four(after(normed, pair))
     products = (
         lax.dot_general(gated, cot_whole, contract_first, preferred_element_type=f32).astype(bf16),
         lax.dot_general(normed, gate_grad, contract_first, preferred_element_type=f32).astype(bf16),
@@ -1002,8 +1103,16 @@
     out_sum, gate_sum = lax.psum(products, "wide")
     whole = whole_ext[:rows].astype(f32)
     wide_place = lax.axis_index("wide").astype(jnp.int32)
-
-    def after_forward(pair):
+    four_place = (wide_place & 3)[None]
+
+    def narrow_halves(array):
+        low, high = array[:, :features], array[:, features:]
+        return jnp.where(right_half, high, low), jnp.where(right_half, low, high)
+
+    def after_forward(products):
+        out_part = jnp.dot(gated, out_weight, preferred_element_type=f32)
+        out_mine, out_other = narrow_halves(out_part)
+        out_theirs = swapped(out_other, "narrow", 1)
         act_grad, select_grad, scan_small = scan_backward(
             selected,
             other_selected,
@@ -1015,16 +1124,15 @@
             masks,
             decay_log,
             entry,
-            tail,
+            passed,
+            returning,
             skip_gain[None],
             step_weight,
-            [normed_four, *products],
         )
-        other_select_grad = swapped(select_grad, "narrow", 1)
-
+        layer_out = (tokens.astype(f32) + (out_mine + out_theirs)).astype(bf16)
         inner_main, edges, conv_small = convolve_grad(
             select_grad,
-            other_select_grad,
+            swapped(select_grad, "narrow", 1),
             select_weight,
             act_grad,
             convolved,
@@ -1032,32 +1140,41 @@
             projected,
             conv_weight,
             masks,
+            out_theirs,
         )
         from_next = passed_along(edges[:8], "wide", -1)
         last_rows = edges[8:] + jnp.where(same_as_last, from_next, 0.0)
         inner_grad = jnp.concatenate([inner_main[: rows - 8], last_rows.astype(bf16)])
+        near = swapped(inner_grad, "wide", 2)
+        far = swapped(inner_grad, "wide", 1)
         normed_part = jnp.einsum(
             "cte,dce->td", jnp.stack([inner_grad, gate_grad]), in_weight, preferred_element_type=f32
         )
         gain_part = jnp.sum(normed_part * whole * inverse, axis=0, keepdims=True)
-        row_part = jnp.sum(normed_part * norm_gain * whole, axis=1, keepdims=True)
-
-        gain_sum = gain_part + swapped(gain_part, "narrow", 1)
-        spare = -(scan_small.shape[0] + conv_small.shape[0] + 1) % 256
-        small = jnp.concatenate(
-            [scan_small, conv_small, gain_sum, jnp.zeros((spare, gain_sum.shape[1]), f32)]
+        row_part = jnp.sum(normed_part * norm_gain * whole, axis=1)[None]
+        keep, sends = small_quarters(
+            four_place, scan_small, conv_small, gain_part, swapped(gain_part, "narrow", 1)
         )
-        small_piece = scattered(small, (1, 2))
-        near = swapped(inner_grad, "wide", 2)
+        smalls = [keep] + [swapped(sends[n - 1], "wide", n) for n in (1, 2, 3)]
+        normed_mine, normed_other = narrow_halves(normed_part)
+        row_theirs = swapped(row_part, "narrow", 1)
+        normed_theirs = swapped(normed_other, "narrow", 1)
         keep, sends = inner_quarter(
             (wide_place >> 2 & 3)[None],
             inner_grad,
             near,
-            swapped(inner_grad, "wide", 1),
-            swapped(near, "wide", 1),
+            far,
+            swapped(after(near, sends), "wide", 1),
             normed_four,
-            small_piece,
+            smalls,
+            [row_theirs],
         )
+        row_sum = (row_part + row_theirs).reshape(rows, 1)
+        gain_mine = jnp.where(right_half, norm_gain[features:], norm_gain[:features])
+        whole_grad = inverse * (gain_mine * (normed_mine + normed_theirs)) - tokens.astype(f32) * (
+            inverse * inverse * inverse
+        ) * (row_sum / (2 * features))
+        tokens_grad = (whole_grad + cotangent.astype(f32)).astype(bf16)
         first_bits, *more_bits = group_bits(2)
         held = keep
         for n, flip in enumerate(flips(first_bits)[1:]):
@@ -1067,33 +1184,15 @@
         held = held.astype(bf16)
         for bits in reversed(group_bits(2)):
             held = gathered(held, bits)
-        return held, normed_part, row_part
-
-    kinds = jax.eval_shape(after_forward, pair)
-    held, normed_part, row_part = lax.cond(
+        return held, layer_out, tokens_grad
+
+    kinds = jax.eval_shape(after_forward, products)
+    held, layer_out, tokens_grad = lax.cond(
         segment_ids[0] >= 0,
         after_forward,
         lambda pair: jax.tree.map(lambda kind: jnp.zeros(kind.shape, kind.dtype), kinds),
-        pair,
-    )
-
-    def narrow_halves(array):
-        low, high = array[:, :features], array[:, features:]
-        return jnp.where(right_half, high, low), jnp.where(right_half, low, high)
-
-    out_part = jnp.dot(gated, out_weight, preferred_element_type=f32)
-    out_mine, out_other = narrow_halves(out_part)
-    out_total = out_mine + swapped(out_other, "narrow", 1)
-    layer_out = (tokens.astype(f32) + out_total).astype(bf16)
-
-    normed_mine, normed_other = narrow_halves(normed_part)
-    row_sum = row_part + swapped(row_part, "narrow", 1)
-    normed_sum = normed_mine + swapped(normed_other, "narrow", 1)
-    gain_mine = jnp.where(right_half, norm_gain[features:], norm_gain[:features])
-    whole_grad = inverse * (gain_mine * normed_sum) - tokens.astype(f32) * (
-        inverse * inverse * inverse
-    ) * (row_sum / (2 * features))
-    tokens_grad = (whole_grad + cotangent.astype(f32)).astype(bf16)
+        products,
+    )
 
     out_weight_grad = out_sum.astype(f32)
     near = swapped(held, "wide", 2)
@@ -1101,12 +1200,7 @@
     results = []
     for flip, quarter in enumerate(quarters):
         results = joined(
-            (wide_place & 3)[None],
-            flip,
-            gate_sum,
-            quarter,
-            results,
-            [layer_out, tokens_grad] if flip == 1 else [],
+            four_place, flip, gate_sum, quarter, results, [] if flip else [out_weight_grad]
         )
     in_weight_grad, small_sum = results
     conv_at = rank + count + 16

time: 285 us -> 272 us (0.954)
  other arithmetic: 31.6 us -> 14.1 us
  Pallas kernels: 70.9 us -> 76 us
    add x9 -> x0, other arithmetic: 9.92 us -> none  [the longest x2 2.69 us: carried(): adjoint = early[1] + through(early[2]) * late[1]]
    pallas_call x0 -> x5, Pallas kernels: none -> 5.81 us  [the longest x2 3.69 us: carried(): pl.pallas_call(round_kernel, in_specs=[pl.BlockSpec(memory_space=pltpu.SM...]
  transfers between devices with their start and end apart: 34 -> 34, of which waited for: 17 -> 20; matrix products, arithmetic and copies ran while one was open for 20% -> 12% of each run, Pallas kernels for 20% -> 18%
where the time goes in v8:
time: 272 us; the launch traced here: 271 us
  waiting for transfers between devices  87.3 us (32%)
  Pallas kernels  76 us (28%)
  starting transfers between devices  44.6 us (16%)
  local copies, waits for them, and re-layouts  18.5 us (7%)
  matrix products  15.2 us (6%)
  between operations  15 us (6%)
  other arithmetic  14.1 us (5%)
    ppermute x28, waiting for transfers between devices, swapped(): return lax.ppermute(array, axis, [(i, i ^ bit) for i in range(peers)])  85.3 us
    pallas_call x5, Pallas kernels, call(): pl.pallas_call(kernel, grid=(width // scan_width,), in_specs=in_specs, ou...  50.1 us
    ppermute x28, starting transfers between devices, swapped(): return lax.ppermute(array, axis, [(i, i ^ bit) for i in range(peers)])  32.6 us
    pallas_call x4, Pallas kernels, joined(): pl.pallas_call(join_kernel, grid_spec=pltpu.PrefetchScalarGridSpec(num_sc...  10.6 us
    ppermute x4, starting transfers between devices, passed_along(): return lax.ppermute(array, axis, pairs)  7.9 us
  transfers between devices with their start and end apart: 34, of which 20 were waited for; matrix products, arithmetic and copies ran while one was open for 12% of the time, Pallas kernels for 18%

profile of v8, /device:TPU:0, one launch (start us, length us, event | category | flops | bytes accessed | tf_op | source)
XLA Modules:
  0.0 271.1 jit_solution(2284297127955839880)
XLA Ops:
  7.2 3.0 %collective-permute-start.18 = (bf16[256,512]{1,0:T(8,128)(2,1)}, bf16[256,512]{1,0:T(8,128)(2,1)S(1)}, u32[]{:S(2)}, u32[]{:S(2)}) collective-permute-start(bf16[256,512]{1,0:T(8,128)(2,1)} %own_ref.1), channel_id=1, source_target_pairs={{0,1},{1,0},{2,3},{3,2},{4,5},{5,4},{6,7},{7,6},{8,9},{9,8},{10,11... | collective-permute-start | bytes 786440 | tf_op jit(solution)/shard_map/ppermute | solution.py:33
  10.3 1.4 edge_rows.1
  11.6 1.4 collective-permute-start.19
  13.1 4.1 %collective-permute-start.20 = (bf16[16,512]{1,0:T(8,128)(2,1)}, bf16[16,512]{1,0:T(8,128)(2,1)S(1)}, u32[]{:S(2)}, u32[]{:S(2)}) collective-permute-start(bf16[16,512]{1,0:T(8,128)(2,1)} %edge_rows.1), channel_id=1, source_target_pairs={{0,3},{1,2},{2,5},{3,4},{4,7},{5,6},{6,9},{7,8},{8,11},{9,10},{10,... | collective-permute-start | bytes 49160 | tf_op jit(solution)/shard_map/ppermute | solution.py:51
  17.2 1.6 collective-permute-start.22
  19.5 2.4 normalized.1
  21.9 4.0 %fusion.20.inner_ref.gate_ref = bf16[2,272,1024]{2,1,0:T(8,128)(2,1)S(1)} fusion(bf16[1024,2,1024]{2,1,0:T(2,128)(2,1)} %param.17, bf16[272,1024]{1,0:T(8,128)(2,1)} %get-tuple-element.157), kind=kOutput, calls=%fused_computation.46 | convolution fusion | flops 1141407744 | bytes 5865472 | tf_op jit(solution)/shard_map/td,dce->cte/dot_general | solution.py:1060
  25.9 3.1 %convolve.1 = (f32[256,1024]{1,0:T(8,128)}, bf16[256,1024]{1,0:T(8,128)(2,1)S(1)}, f32[96,256]{1,0:T(8,128)S(1)}) custom-call(bf16[2,272,1024]{2,1,0:T(8,128)(2,1)S(1)} %fusion.20.inner_ref.gate_ref, f32[4,1024]{1,0:T(4,128)S(1)} %copy-done.37, f32[1,1024]{1,0:T(1,128)} %bitcast.64, bf16[96,1024]{1,0:T(8,128)(2,1)S(1)} %copy-done.22, ...), custom_call_target="tpu_custom_call" | custom-call | flops 1 | bytes 1 | tf_op jit(solution)/shard_map/convolve/pallas_call | solution.py:129
  29.1 1.5 collective-permute-start.21
  31.4 2.6 collective-permute-done.21.other_ref
  34.7 9.9 %scan_ends.1 = (f32[256,1024]{1,0:T(8,128)}, f32[256,1024]{1,0:T(8,128)}, f32[40,1024]{1,0:T(8,128)}) custom-call(f32[96,256]{1,0:T(8,128)S(1)} %get-tuple-element.159.selected_ref, f32[96,256]{1,0:T(8,128)S(1)} %collective-permute-done.21.other_ref, bf16[64,1024]{1,0:T(8,128)(2,1)S(1)} %copy-done.28, f32[1,1024]{1,0:T(1,128)} %bitcast.65, ...), custom_call_target="tpu_custom_call" | custom-call | flops 1 | bytes 1 | tf_op jit(solution)/shard_map/scan_ends/pallas_call | solution.py:129
  45.1 1.4 collective-permute-done.23.other_ref
  47.2 1.8 carry_round.2
  49.0 2.8 %collective-permute-start.24 = (f32[40,1024]{1,0:T(8,128)}, f32[40,1024]{1,0:T(8,128)}, u32[]{:S(2)}, u32[]{:S(2)}) collective-permute-start(f32[40,1024]{1,0:T(8,128)} %get-tuple-element.164.own_ref), channel_id=1, source_target_pairs={{0,4},{2,6},{4,0},{6,2},{8,12},{10,14},{12,8},{14,10},{16,20},{18,... | collective-permute-start | bytes 491528 | tf_op jit(solution)/shard_map/ppermute | solution.py:33
  51.8 4.8 %collective-permute-done.24.other_ref = f32[40,1024]{1,0:T(8,128)} collective-permute-done((f32[40,1024]{1,0:T(8,128)}, f32[40,1024]{1,0:T(8,128)}, u32[]{:S(2)}, u32[]{:S(2)}) %collective-permute-start.24) | collective-permute-done | bytes 163872 | tf_op jit(solution)/shard_map/ppermute | solution.py:33
  56.6 1.8 carry_round.3
  58.5 1.5 fusion.31
  60.0 3.9 %collective-permute-start.25 = (f32[16,1024]{1,0:T(8,128)S(1)}, f32[16,1024]{1,0:T(8,128)S(1)}, u32[]{:S(2)}, u32[]{:S(2)}) collective-permute-start(f32[16,1024]{1,0:T(8,128)S(1)} %get-tuple-element.253), channel_id=1, source_target_pairs={{0,8},{2,10},{4,12},{6,14},{8,16},{10,18},{12,20},{14,22},{16,24},... | collective-permute-start | bytes 196616 | tf_op jit(solution)/shard_map/ppermute | solution.py:28
  63.9 1.9 collective-permute-done.25.entering_ref
  66.4 9.8 %scan_forward.1 = (bf16[2,256,1024]{2,1,0:T(8,128)(2,1)}, f32[16,1024]{1,0:T(8,128)}) custom-call(f32[96,256]{1,0:T(8,128)S(1)} %get-tuple-element.159.selected_ref, f32[96,256]{1,0:T(8,128)} %copy-done.20, f32[256,1024]{1,0:T(8,128)} %get-tuple-element.162.step_ref, bf16[256,1024]{1,0:T(8,128)(2,1)S(1)} %get-tuple-element.160.act_ref, ...), custom_call_target="tpu_custom_call" | custom-call | flops 1 | bytes 1 | tf_op jit(solution)/shard_map/scan_forward/pallas_call | solution.py:129
  76.2 3.2 %convolution_convert_fusion.1 = bf16[1024,1024]{1,0:T(8,128)(2,1)} fusion(bf16[272,1024]{1,0:T(8,128)(2,1)S(1)} %copy-done.13, bf16[2,256,1024]{2,1,0:T(8,128)(2,1)} %get-tuple-element.169.refs_1_), kind=kOutput, calls=%fused_computation.44 | convolution fusion | flops 537919488 | bytes 3145728 | tf_op jit(solution)/shard_map/dot_general | solution.py:1101
  79.4 2.1 convolution_convert_fusion
  84.2 2.3 slice_convert_fusion
  86.6 1.3 collective-permute-start.26
  88.0 1.3 dynamic-slice_bitcast_fusion
  89.3 1.4 collective-permute-start.27
  92.3 6.1 %collective-permute-done.27 = bf16[256,256]{1,0:T(8,128)(2,1)S(1)} collective-permute-done((bf16[256,256]{1,0:T(8,128)(2,1)S(1)}, bf16[256,256]{1,0:T(8,128)(2,1)S(1)}, u32[]{:S(2)}, u32[]{:S(2)}) %collective-permute-start.27) | collective-permute-done | bytes 131104 | tf_op jit(solution)/shard_map/ppermute | solution.py:33
  98.5 2.2 collective-permute-done.29
  101.6 127.9 %conditional.1 = (bf16[320,1024]{1,0:T(8,128)(2,1)}, bf16[256,512]{1,0:T(8,128)(2,1)}, bf16[256,512]{1,0:T(8,128)(2,1)}) conditional(s32[]{:T(128)} %bitcast.16, () %tuple.16, (s32[]{:T(128)}, f32[1024]{0:T(1024)S(1)}, f32[96,256]{1,0:T(8,128)S(1)}, f32[96,256]{1,0:T(8,128)S(1)}, f32[256,1024]{1,0:T(8,128)}, /*index=5*/f32[256,1024]{1,0:T(8,128)S(1)}, ...), branch_computations={%region_0.1_spmd, %region_1.4_spmd} | conditional | flops 1619861760 | bytes 68363624 | solution.py:1190
  103.4 1.7 collective-permute-start.1
  105.1 23.3 %scan_backward.1 = (f32[256,1024]{1,0:T(8,128)}, f32[96,256]{1,0:T(8,128)}, f32[96,1024]{1,0:T(8,128)}) custom-call(f32[96,256]{1,0:T(8,128)S(1)} %get-tuple-element.70.selected_ref, f32[96,256]{1,0:T(8,128)S(1)} %get-tuple-element.71.other_ref, f32[256,1024]{1,0:T(8,128)S(1)} %copy-done.16, f32[256,1024]{1,0:T(8,128)S(1)} %get-tuple-element.73.step_ref, ...), custom_call_target="tpu_custom_call" | custom-call | flops 1 | bytes 1 | tf_op jit(solution)/shard_map/cond/branch_1_fun/scan_backward/pallas_call | solution.py:129
  129.5 4.3 %collective-permute-done.other_ref = f32[96,256]{1,0:T(8,128)S(1)} collective-permute-done((f32[96,256]{1,0:T(8,128)}, f32[96,256]{1,0:T(8,128)S(1)}, u32[]{:S(2)}, u32[]{:S(2)}) %collective-permute-start) | collective-permute-done | bytes 98336 | tf_op jit(solution)/shard_map/cond/branch_1_fun/ppermute | solution.py:33
  134.7 4.0 %convolve_grad.1 = (bf16[256,1024]{1,0:T(8,128)(2,1)}, f32[16,1024]{1,0:T(8,128)}, f32[112,1024]{1,0:T(8,128)}) custom-call(f32[96,256]{1,0:T(8,128)} %get-tuple-element.84.select_grad_ref, f32[96,256]{1,0:T(8,128)} %copy-done.34, bf16[96,1024]{1,0:T(8,128)(2,1)S(1)} %get-tuple-element.85.select_ref, f32[256,1024]{1,0:T(8,128)} %get-tuple-element.86.act_grad_ref, ...), custom_call_target="tpu_custom_call" | custom-call | flops 1 | bytes 1 | tf_op jit(solution)/shard_map/cond/branch_1_fun/convolve_grad/pallas_call | solution.py:129
  139.4 1.3 collective-permute-start.2
  141.5 1.1 slice.52
  143.7 2.9 %collective-permute-start.3 = (bf16[256,1024]{1,0:T(8,128)(2,1)S(1)}, bf16[256,1024]{1,0:T(8,128)(2,1)S(1)}, u32[]{:S(2)}, u32[]{:S(2)}) collective-permute-start(bf16[256,1024]{1,0:T(8,128)(2,1)S(1)} %get-tuple-element.230.own_ref), channel_id=1, source_target_pairs={{0,4},{2,6},{4,0},{6,2},{8,12},{10,14},{12,8},{14,10},{16,20},{18,... | collective-permute-start | bytes 1572872 | tf_op jit(solution)/shard_map/cond/branch_1_fun/ppermute | solution.py:33
  146.6 4.5 %multiply_reduce_fusion = (f32[256]{0:T(256)S(1)}, f32[1024]{0:T(1024)S(1)}, f32[256,1024]{1,0:T(8,128)S(1)}) fusion(f32[256,1024]{1,0:T(8,128)} %get-tuple-element.100, f32[1024]{0:T(1024)S(1)} %get-tuple-element.105, f32[256]{0:T(256)S(1)} %bitcast.62, bf16[1024,2,1024]{2,1,0:T(2,128)(2,1)} %get-tuple-element.215, ...), kind=kOutput, calls=%fused_computation.6 | convolution fusion | flops 1075837696 | bytes 7350272 | tf_op jit(solution)/shard_map/cond/branch_1_fun/cte,dce->td/dot_general | solution.py:1150
  151.7 1.3 collective-permute-start.4
  153.1 1.7 collective-permute-done.5.other_gain_ref
  155.3 2.1 small_quarters.1
  157.4 3.5 %collective-permute-done.3.near_ref = bf16[256,1024]{1,0:T(8,128)(2,1)S(1)} collective-permute-done((bf16[256,1024]{1,0:T(8,128)(2,1)S(1)}, bf16[256,1024]{1,0:T(8,128)(2,1)S(1)}, u32[]{:S(2)}, u32[]{:S(2)}) %collective-permute-start.3) | collective-permute-done | bytes 524320 | tf_op jit(solution)/shard_map/cond/branch_1_fun/ppermute | solution.py:33
  162.7 1.5 collective-permute-start.10
  164.2 1.1 slice_bitcast_fusion.3
  168.0 6.4 %collective-permute-done.8.second_ref = bf16[64,1024]{1,0:T(8,128)(2,1)S(1)} collective-permute-done((bf16[64,1024]{1,0:T(8,128)(2,1)S(1)}, bf16[64,1024]{1,0:T(8,128)(2,1)S(1)}, u32[]{:S(2)}, u32[]{:S(2)}) %collective-permute-start.8) | collective-permute-done | bytes 131104 | tf_op jit(solution)/shard_map/cond/branch_1_fun/ppermute | solution.py:33
  174.4 4.8 %collective-permute-done.9.third_ref = bf16[64,1024]{1,0:T(8,128)(2,1)S(1)} collective-permute-done((bf16[64,1024]{1,0:T(8,128)(2,1)S(1)}, bf16[64,1024]{1,0:T(8,128)(2,1)S(1)}, u32[]{:S(2)}, u32[]{:S(2)}) %collective-permute-start.9) | collective-permute-done | bytes 131104 | tf_op jit(solution)/shard_map/cond/branch_1_fun/ppermute | solution.py:33
  179.9 3.5 %inner_quarter.1 = (f32[80,1024]{1,0:T(8,128)}, bf16[3,80,1024]{2,1,0:T(8,128)(2,1)}) custom-call(s32[1]{0:T(128)} %bitcast.place_ref, bf16[256,1024]{1,0:T(8,128)(2,1)} %copy-done.8, bf16[256,1024]{1,0:T(8,128)(2,1)} %copy-done.10, bf16[256,1024]{1,0:T(8,128)(2,1)} %collective-permute-done.4.far_ref, bf16[256,1024]{1,0:T(8,128)(2,1)} %collective-permute-done.6.last_ref, ...), custom_call_target="tpu_custom_call" | custom-call | flops 1 | bytes 1 | tf_op jit(solution)/shard_map/cond/branch_1_fun/inner_quarter/pallas_call | solution.py:899
  183.4 1.1 slice_bitcast_fusion.2
  184.6 1.7 collective-permute-start.11
  186.2 2.3 collective-permute-start.12
  189.7 8.6 %collective-permute-done.11 = bf16[80,1024]{1,0:T(8,128)(2,1)S(1)} collective-permute-done((bf16[80,1024]{1,0:T(8,128)(2,1)S(1)}, bf16[80,1024]{1,0:T(8,128)(2,1)S(1)}, u32[]{:S(2)}, u32[]{:S(2)}) %collective-permute-start.11) | collective-permute-done | bytes 163872 | tf_op jit(solution)/shard_map/cond/branch_1_fun/ppermute | solution.py:33
  198.5 8.1 %collective-permute-done.13 = bf16[80,1024]{1,0:T(8,128)(2,1)S(1)} collective-permute-done((bf16[80,1024]{1,0:T(8,128)(2,1)S(1)}, bf16[80,1024]{1,0:T(8,128)(2,1)S(1)}, u32[]{:S(2)}, u32[]{:S(2)}) %collective-permute-start.13) | collective-permute-done | bytes 163872 | tf_op jit(solution)/shard_map/cond/branch_1_fun/ppermute | solution.py:33
  206.6 1.1 add_convert_fusion
  207.6 3.7 %collective-permute-start.16 = (bf16[80,1024]{1,0:T(8,128)(2,1)S(1)}, bf16[80,1024]{1,0:T(8,128)(2,1)S(1)}, u32[]{:S(2)}, u32[]{:S(2)}) collective-permute-start(bf16[80,1024]{1,0:T(8,128)(2,1)S(1)} %add_convert_fusion), channel_id=1, source_target_pairs={{0,8},{2,10},{4,12},{6,14},{8,0},{10,2},{12,4},{14,6},{16,24},{18,... | collective-permute-start | bytes 491528 | tf_op jit(solution)/shard_map/cond/branch_1_fun/ppermute | solution.py:33
  212.4 1.4 collective-permute-start.14
  213.9 2.1 collective-permute-done.16
  216.0 5.4 %collective-permute-done.14 = bf16[80,1024]{1,0:T(8,128)(2,1)S(1)} collective-permute-done((bf16[80,1024]{1,0:T(8,128)(2,1)S(1)}, bf16[80,1024]{1,0:T(8,128)(2,1)S(1)}, u32[]{:S(2)}, u32[]{:S(2)}) %collective-permute-start.14) | collective-permute-done | bytes 163872 | tf_op jit(solution)/shard_map/cond/branch_1_fun/ppermute | solution.py:33
  221.4 7.0 %collective-permute-done.15 = bf16[80,1024]{1,0:T(8,128)(2,1)S(1)} collective-permute-done((bf16[80,1024]{1,0:T(8,128)(2,1)S(1)}, bf16[80,1024]{1,0:T(8,128)(2,1)S(1)}, u32[]{:S(2)}, u32[]{:S(2)}) %collective-permute-start.15) | collective-permute-done | bytes 163872 | tf_op jit(solution)/shard_map/cond/branch_1_fun/ppermute | solution.py:33
  229.7 15.8 %collective-permute-done.30.inner_ref = bf16[320,1024]{1,0:T(8,128)(2,1)S(1)} collective-permute-done((bf16[320,1024]{1,0:T(8,128)(2,1)}, bf16[320,1024]{1,0:T(8,128)(2,1)S(1)}, u32[]{:S(2)}, u32[]{:S(2)}) %collective-permute-start.30) | collective-permute-done | bytes 655392 | tf_op jit(solution)/shard_map/ppermute | solution.py:33
  245.5 4.3 %convert_element_type.58.rest_0_ = f32[1024,1024]{1,0:T(8,128)} convert(bf16[1024,1024]{1,0:T(8,128)(2,1)} %get-tuple-element.226) | non-fusion elementwise | flops 1048576 | bytes 6291456 | tf_op jit(solution)/shard_map/convert_element_type | solution.py:1197
  249.8 2.6 joined.4
  253.3 2.7 joined.5
  256.0 2.7 joined.6
  259.5 2.7 joined.7
  262.1 2.1 small_parts.1
  (153 shorter events, 26.5 us)
Async XLA Ops:
  7.2 238.3 %all-reduce.3.cloned.1.call-start = ((), (), s32[]{:S(2)}) async-start(), calls=%async_computation | async-start | bytes 8388608 | tf_op jit(solution)/shard_map/psum | solution.py:1103
  7.2 11.6 %collective-permute-start.18 = (bf16[256,512]{1,0:T(8,128)(2,1)}, bf16[256,512]{1,0:T(8,128)(2,1)S(1)}, u32[]{:S(2)}, u32[]{:S(2)}) collective-permute-start(bf16[256,512]{1,0:T(8,128)(2,1)} %own_ref.1), channel_id=1, source_target_pairs={{0,1},{1,0},{2,3},{3,2},{4,5},{5,4},{6,7},{7,6},{8,9},{9,8},{10,11... | collective-permute-start | bytes 786440 | tf_op jit(solution)/shard_map/ppermute | solution.py:33
  11.6 7.1 %collective-permute-start.19 = (bf16[16,512]{1,0:T(8,128)(2,1)}, bf16[16,512]{1,0:T(8,128)(2,1)S(1)}, u32[]{:S(2)}, u32[]{:S(2)}) collective-permute-start(bf16[16,512]{1,0:T(8,128)(2,1)} %edge_rows.1), channel_id=1, source_target_pairs={{0,2},{2,4},{4,6},{6,8},{8,10},{10,12},{12,14},{14,16},{16,18},{18... | collective-permute-start | bytes 49160 | tf_op jit(solution)/shard_map/ppermute | solution.py:28
  13.1 5.7 %collective-permute-start.20 = (bf16[16,512]{1,0:T(8,128)(2,1)}, bf16[16,512]{1,0:T(8,128)(2,1)S(1)}, u32[]{:S(2)}, u32[]{:S(2)}) collective-permute-start(bf16[16,512]{1,0:T(8,128)(2,1)} %edge_rows.1), channel_id=1, source_target_pairs={{0,3},{1,2},{2,5},{3,4},{4,7},{5,6},{6,9},{7,8},{8,11},{9,10},{10,... | collective-permute-start | bytes 49160 | tf_op jit(solution)/shard_map/ppermute | solution.py:51
  17.2 13.4 %collective-permute-start.22 = (bf16[256,512]{1,0:T(8,128)(2,1)}, bf16[256,512]{1,0:T(8,128)(2,1)S(1)}, u32[]{:S(2)}, u32[]{:S(2)}) collective-permute-start(bf16[256,512]{1,0:T(8,128)(2,1)} %param.27), channel_id=1, source_target_pairs={{0,1},{1,0},{2,3},{3,2},{4,5},{5,4},{6,7},{7,6},{8,9},{9,8},{10,11... | collective-permute-start | bytes 786440 | tf_op jit(solution)/shard_map/ppermute | solution.py:33
  21.9 4.0 %copy-start.22 = (bf16[96,1024]{1,0:T(8,128)(2,1)S(1)}, bf16[96,1024]{1,0:T(8,128)(2,1)}, u32[]{:S(2)}) copy-start(bf16[96,1024]{1,0:T(8,128)(2,1)} %select_ref.1) | copy-start | bytes 589828
  21.9 4.0 %copy-start.37 = (f32[4,1024]{1,0:T(4,128)S(1)}, f32[4,1024]{1,0:T(4,128)}, u32[]{:S(2)}) copy-start(f32[4,1024]{1,0:T(4,128)} %conv_weight_ref.1) | copy-start | bytes 49156
  21.9 8.7 %copy-start.17 = (bf16[256,512]{1,0:T(8,128)(2,1)S(1)}, bf16[256,512]{1,0:T(8,128)(2,1)}, u32[]{:S(2)}) copy-start(bf16[256,512]{1,0:T(8,128)(2,1)} %param.27) | copy-start | bytes 786436
  25.9 4.8 %copy-start.4 = (bf16[1024,1024]{1,0:T(8,128)(2,1)S(1)}, bf16[1024,1024]{1,0:T(8,128)(2,1)}, u32[]{:S(2)}) copy-start(bf16[1024,1024]{1,0:T(8,128)(2,1)} %param.25) | copy-start | bytes 6291460
  29.1 36.7 %copy-start.2 = (bf16[256,1024]{1,0:T(8,128)(2,1)}, bf16[256,1024]{1,0:T(8,128)(2,1)S(1)}, u32[]{:S(2)}) copy-start(bf16[256,1024]{1,0:T(8,128)(2,1)S(1)} %get-tuple-element.160.act_ref) | copy-start | bytes 1572868
  29.1 5.0 %collective-permute-start.21 = (f32[96,256]{1,0:T(8,128)S(1)}, f32[96,256]{1,0:T(8,128)S(1)}, u32[]{:S(2)}, u32[]{:S(2)}) collective-permute-start(f32[96,256]{1,0:T(8,128)S(1)} %get-tuple-element.159.selected_ref), channel_id=1, source_target_pairs={{0,1},{1,0},{2,3},{3,2},{4,5},{5,4},{6,7},{7,6},{8,9},{9,8},{10,11... | collective-permute-start | bytes 294920 | tf_op jit(solution)/shard_map/ppermute | solution.py:33
  30.6 4.0 %copy-start.15 = (f32[16,1024]{1,0:T(8,128)S(1)}, f32[16,1024]{1,0:T(8,128)}, u32[]{:S(2)}) copy-start(f32[16,1024]{1,0:T(8,128)} %decay_log_ref.7) | copy-start | bytes 196612
  30.6 4.0 %copy-start.28 = (bf16[64,1024]{1,0:T(8,128)(2,1)S(1)}, bf16[64,1024]{1,0:T(8,128)(2,1)}, u32[]{:S(2)}) copy-start(bf16[64,1024]{1,0:T(8,128)(2,1)} %step_weight_ref.1) | copy-start | bytes 393220
  34.7 31.7 %copy-start.38 = (f32[1024]{0:T(1024)S(1)}, f32[1024]{0:T(1024)}, u32[]{:S(2)}) copy-start(f32[1024]{0:T(1024)} %param.24) | copy-start | bytes 12292
  44.6 1.9 collective-permute-start.23
  49.0 7.6 %collective-permute-start.24 = (f32[40,1024]{1,0:T(8,128)}, f32[40,1024]{1,0:T(8,128)}, u32[]{:S(2)}, u32[]{:S(2)}) collective-permute-start(f32[40,1024]{1,0:T(8,128)} %get-tuple-element.164.own_ref), channel_id=1, source_target_pairs={{0,4},{2,6},{4,0},{6,2},{8,12},{10,14},{12,8},{14,10},{16,20},{18,... | collective-permute-start | bytes 491528 | tf_op jit(solution)/shard_map/ppermute | solution.py:33
  60.0 5.8 %collective-permute-start.25 = (f32[16,1024]{1,0:T(8,128)S(1)}, f32[16,1024]{1,0:T(8,128)S(1)}, u32[]{:S(2)}, u32[]{:S(2)}) collective-permute-start(f32[16,1024]{1,0:T(8,128)S(1)} %get-tuple-element.253), channel_id=1, source_target_pairs={{0,8},{2,10},{4,12},{6,14},{8,16},{10,18},{12,20},{14,22},{16,24},... | collective-permute-start | bytes 196616 | tf_op jit(solution)/shard_map/ppermute | solution.py:28
  66.4 9.8 %copy-start.13 = (bf16[272,1024]{1,0:T(8,128)(2,1)S(1)}, bf16[272,1024]{1,0:T(8,128)(2,1)}, u32[]{:S(2)}) copy-start(bf16[272,1024]{1,0:T(8,128)(2,1)} %get-tuple-element.157) | copy-start | bytes 1671172
  84.2 7.2 %copy-start.1 = (bf16[2,256,1024]{2,1,0:T(8,128)(2,1)S(1)}, bf16[2,256,1024]{2,1,0:T(8,128)(2,1)}, u32[]{:S(2)}) copy-start(bf16[2,256,1024]{2,1,0:T(8,128)(2,1)} %get-tuple-element.169.refs_1_) | copy-start | bytes 3145732
  86.6 15.0 %collective-permute-start.26 = (f32[16,1024]{1,0:T(8,128)}, f32[16,1024]{1,0:T(8,128)}, u32[]{:S(2)}, u32[]{:S(2)}) collective-permute-start(f32[16,1024]{1,0:T(8,128)} %get-tuple-element.252), channel_id=1, source_target_pairs={{8,0},{10,2},{12,4},{14,6},{16,8},{18,10},{20,12},{22,14},{24,16},... | collective-permute-start | bytes 196616 | tf_op jit(solution)/shard_map/ppermute | solution.py:28
  87.9 13.7 %copy-start.3 = (bf16[256,1024]{1,0:T(8,128)(2,1)S(1)}, bf16[256,1024]{1,0:T(8,128)(2,1)}, u32[]{:S(2)}) copy-start(bf16[256,1024]{1,0:T(8,128)(2,1)} %copy-done.2) | copy-start | bytes 1572868
  87.9 13.7 %copy-start.5 = (bf16[1024,1024]{1,0:T(8,128)(2,1)S(1)}, bf16[1024,1024]{1,0:T(8,128)(2,1)}, u32[]{:S(2)}) copy-start(bf16[1024,1024]{1,0:T(8,128)(2,1)} %param.25) | copy-start | bytes 6291460
  87.9 13.7 %copy-start.6 = (f32[256,1024]{1,0:T(8,128)S(1)}, f32[256,1024]{1,0:T(8,128)}, u32[]{:S(2)}) copy-start(f32[256,1024]{1,0:T(8,128)} %get-tuple-element.162.step_ref) | copy-start | bytes 3145732
  87.9 13.7 %copy-start.21 = (f32[96,256]{1,0:T(8,128)S(1)}, f32[96,256]{1,0:T(8,128)}, u32[]{:S(2)}) copy-start(f32[96,256]{1,0:T(8,128)} %copy-done.20) | copy-start | bytes 294916
  87.9 13.7 %copy-start.23 = (bf16[96,1024]{1,0:T(8,128)(2,1)S(1)}, bf16[96,1024]{1,0:T(8,128)(2,1)}, u32[]{:S(2)}) copy-start(bf16[96,1024]{1,0:T(8,128)(2,1)} %select_ref.1) | copy-start | bytes 589828
  87.9 13.7 %copy-start.27 = (f32[40,1024]{1,0:T(8,128)S(1)}, f32[40,1024]{1,0:T(8,128)}, u32[]{:S(2)}) copy-start(f32[40,1024]{1,0:T(8,128)} %get-tuple-element.166.passed_ref) | copy-start | bytes 491524
  87.9 13.7 %copy-start.35 = (f32[16,1024]{1,0:T(8,128)S(1)}, f32[16,1024]{1,0:T(8,128)}, u32[]{:S(2)}) copy-start(f32[16,1024]{1,0:T(8,128)} %get-tuple-element.168) | copy-start | bytes 196612
  87.9 13.7 %copy-start.39 = (f32[1024]{0:T(1024)S(1)}, f32[1024]{0:T(1024)}, u32[]{:S(2)}) copy-start(f32[1024]{0:T(1024)} %param.16) | copy-start | bytes 12292
  89.3 9.2 %collective-permute-start.27 = (bf16[256,256]{1,0:T(8,128)(2,1)S(1)}, bf16[256,256]{1,0:T(8,128)(2,1)S(1)}, u32[]{:S(2)}, u32[]{:S(2)}) collective-permute-start(bf16[256,256]{1,0:T(8,128)(2,1)S(1)} %get-tuple-element.249), channel_id=1, source_target_pairs={{0,4},{2,6},{4,0},{6,2},{8,12},{10,14},{12,8},{14,10},{16,20},{18,... | collective-permute-start | bytes 393224 | tf_op jit(solution)/shard_map/ppermute | solution.py:33
  90.7 7.8 %collective-permute-start.28 = (bf16[256,256]{1,0:T(8,128)(2,1)S(1)}, bf16[256,256]{1,0:T(8,128)(2,1)S(1)}, u32[]{:S(2)}, u32[]{:S(2)}) collective-permute-start(bf16[256,256]{1,0:T(8,128)(2,1)S(1)} %get-tuple-element.248), channel_id=1, source_target_pairs={{0,2},{2,0},{4,6},{6,4},{8,10},{10,8},{12,14},{14,12},{16,18},{18,... | collective-permute-start | bytes 393224 | tf_op jit(solution)/shard_map/ppermute | solution.py:33
  90.7 10.0 %collective-permute-start.29 = (bf16[256,256]{1,0:T(8,128)(2,1)S(1)}, bf16[256,256]{1,0:T(8,128)(2,1)S(1)}, u32[]{:S(2)}, u32[]{:S(2)}) collective-permute-start(bf16[256,256]{1,0:T(8,128)(2,1)S(1)} %get-tuple-element.247), channel_id=1, source_target_pairs={{0,6},{2,4},{4,2},{6,0},{8,14},{10,12},{12,10},{14,8},{16,22},{18,... | collective-permute-start | bytes 393224 | tf_op jit(solution)/shard_map/ppermute | solution.py:33
  103.4 30.4 %collective-permute-start.1 = (f32[256,512]{1,0:T(8,128)}, f32[256,512]{1,0:T(8,128)S(1)}, u32[]{:S(2)}, u32[]{:S(2)}) collective-permute-start(f32[256,512]{1,0:T(8,128)} %slice_select_fusion.1), channel_id=1, source_target_pairs={{0,1},{1,0},{2,3},{3,2},{4,5},{5,4},{6,7},{7,6},{8,9},{9,8},{10,11... | collective-permute-start | bytes 1572872 | tf_op jit(solution)/shard_map/cond/branch_1_fun/ppermute | solution.py:33
  105.1 29.6 %copy-start.19 = (f32[256,1024]{1,0:T(8,128)S(1)}, f32[256,1024]{1,0:T(8,128)}, u32[]{:S(2)}) copy-start(f32[256,1024]{1,0:T(8,128)} %get-tuple-element.87.convolved_ref) | copy-start | bytes 3145732 | tf_op jit(solution)/shard_map/cond
  128.4 5.5 %collective-permute-start = (f32[96,256]{1,0:T(8,128)}, f32[96,256]{1,0:T(8,128)S(1)}, u32[]{:S(2)}, u32[]{:S(2)}) collective-permute-start(f32[96,256]{1,0:T(8,128)} %get-tuple-element.84.select_grad_ref), channel_id=1, source_target_pairs={{0,1},{1,0},{2,3},{3,2},{4,5},{5,4},{6,7},{7,6},{8,9},{9,8},{10,11... | collective-permute-start | bytes 294920 | tf_op jit(solution)/shard_map/cond/branch_1_fun/ppermute | solution.py:33
  134.7 6.8 %copy-start.33 = (f32[256,1]{1,0:T(8,128)S(1)}, f32[256,1]{1,0:T(8,128)}, u32[]{:S(2)}) copy-start(f32[256,1]{1,0:T(8,128)} %get-tuple-element.217) | copy-start | bytes 3076 | tf_op jit(solution)/shard_map/cond
  139.4 3.2 %collective-permute-start.2 = (f32[8,1024]{1,0:T(8,128)S(1)}, f32[8,1024]{1,0:T(8,128)S(1)}, u32[]{:S(2)}, u32[]{:S(2)}) collective-permute-start(f32[8,1024]{1,0:T(8,128)S(1)} %slice.56), channel_id=1, source_target_pairs={{2,0},{4,2},{6,4},{8,6},{10,8},{12,10},{14,12},{16,14},{18,16},{20... | collective-permute-start | bytes 98312 | tf_op jit(solution)/shard_map/cond/branch_1_fun/ppermute | solution.py:28
  143.6 8.1 %copy-start.8 = (bf16[256,1024]{1,0:T(8,128)(2,1)}, bf16[256,1024]{1,0:T(8,128)(2,1)S(1)}, u32[]{:S(2)}) copy-start(bf16[256,1024]{1,0:T(8,128)(2,1)S(1)} %get-tuple-element.230.own_ref) | copy-start | bytes 1572868 | tf_op jit(solution)/shard_map/cond
  143.7 17.3 %collective-permute-start.3 = (bf16[256,1024]{1,0:T(8,128)(2,1)S(1)}, bf16[256,1024]{1,0:T(8,128)(2,1)S(1)}, u32[]{:S(2)}, u32[]{:S(2)}) collective-permute-start(bf16[256,1024]{1,0:T(8,128)(2,1)S(1)} %get-tuple-element.230.own_ref), channel_id=1, source_target_pairs={{0,4},{2,6},{4,0},{6,2},{8,12},{10,14},{12,8},{14,10},{16,20},{18,... | collective-permute-start | bytes 1572872 | tf_op jit(solution)/shard_map/cond/branch_1_fun/ppermute | solution.py:33
  151.1 3.7 %copy-start.43 = (f32[1024]{0:T(1024)}, f32[1024]{0:T(1024)S(1)}, u32[]{:S(2)}) copy-start(f32[1024]{0:T(1024)S(1)} %get-tuple-element.224) | copy-start | bytes 12292 | tf_op jit(solution)/shard_map/cond
  151.1 3.7 %collective-permute-start.5 = (f32[1,1024]{1,0:T(1,128)S(1)}, f32[1,1024]{1,0:T(1,128)S(1)}, u32[]{:S(2)}, u32[]{:S(2)}) collective-permute-start(f32[1,1024]{1,0:T(1,128)S(1)} %bitcast.66), channel_id=1, source_target_pairs={{0,1},{1,0},{2,3},{3,2},{4,5},{5,4},{6,7},{7,6},{8,9},{9,8},{10,11... | collective-permute-start | bytes 12296 | tf_op jit(solution)/shard_map/cond/branch_1_fun/ppermute | solution.py:33
  151.7 27.5 %collective-permute-start.4 = (bf16[256,1024]{1,0:T(8,128)(2,1)S(1)}, bf16[256,1024]{1,0:T(8,128)(2,1)}, u32[]{:S(2)}, u32[]{:S(2)}) collective-permute-start(bf16[256,1024]{1,0:T(8,128)(2,1)S(1)} %get-tuple-element.230.own_ref), channel_id=1, source_target_pairs={{0,2},{2,0},{4,6},{6,4},{8,10},{10,8},{12,14},{14,12},{16,18},{18,... | collective-permute-start | bytes 1572872 | tf_op jit(solution)/shard_map/cond/branch_1_fun/ppermute | solution.py:33
  162.5 17.4 %copy-start.9 = (bf16[4,256,256]{2,1,0:T(8,128)(2,1)S(1)}, bf16[4,256,256]{2,1,0:T(8,128)(2,1)}, u32[]{:S(2)}) copy-start(bf16[4,256,256]{2,1,0:T(8,128)(2,1)} %get-tuple-element.103.normed_ref) | copy-start | bytes 1572868 | tf_op jit(solution)/shard_map/cond
  162.5 16.7 %collective-permute-start.6 = (bf16[256,1024]{1,0:T(8,128)(2,1)}, bf16[256,1024]{1,0:T(8,128)(2,1)}, u32[]{:S(2)}, u32[]{:S(2)}) collective-permute-start(bf16[256,1024]{1,0:T(8,128)(2,1)} %after.2), channel_id=1, source_target_pairs={{0,2},{2,0},{4,6},{6,4},{8,10},{10,8},{12,14},{14,12},{16,18},{18,... | collective-permute-start | bytes 1572872 | tf_op jit(solution)/shard_map/cond/branch_1_fun/ppermute | solution.py:33
  162.7 3.6 %collective-permute-start.10 = (f32[1,256]{1,0:T(1,128)S(1)}, f32[1,256]{1,0:T(1,128)S(1)}, u32[]{:S(2)}, u32[]{:S(2)}) collective-permute-start(f32[1,256]{1,0:T(1,128)S(1)} %bitcast.71), channel_id=1, source_target_pairs={{0,1},{1,0},{2,3},{3,2},{4,5},{5,4},{6,7},{7,6},{8,9},{9,8},{10,11... | collective-permute-start | bytes 3080 | tf_op jit(solution)/shard_map/cond/branch_1_fun/ppermute | solution.py:33
  165.4 2.0 collective-permute-start.7
  165.4 9.0 %collective-permute-start.8 = (bf16[64,1024]{1,0:T(8,128)(2,1)S(1)}, bf16[64,1024]{1,0:T(8,128)(2,1)S(1)}, u32[]{:S(2)}, u32[]{:S(2)}) collective-permute-start(bf16[64,1024]{1,0:T(8,128)(2,1)S(1)} %get-tuple-element.235), channel_id=1, source_target_pairs={{0,4},{2,6},{4,0},{6,2},{8,12},{10,14},{12,8},{14,10},{16,20},{18,... | collective-permute-start | bytes 393224 | tf_op jit(solution)/shard_map/cond/branch_1_fun/ppermute | solution.py:33
  166.3 13.0 %copy-start.42 = (f32[1,256]{1,0:T(1,128)}, f32[1,256]{1,0:T(1,128)S(1)}, u32[]{:S(2)}) copy-start(f32[1,256]{1,0:T(1,128)S(1)} %collective-permute-done.10.rest_0_) | copy-start | bytes 3076 | tf_op jit(solution)/shard_map/cond
  166.3 12.9 %collective-permute-start.9 = (bf16[64,1024]{1,0:T(8,128)(2,1)S(1)}, bf16[64,1024]{1,0:T(8,128)(2,1)S(1)}, u32[]{:S(2)}, u32[]{:S(2)}) collective-permute-start(bf16[64,1024]{1,0:T(8,128)(2,1)S(1)} %get-tuple-element.234), channel_id=1, source_target_pairs={{0,6},{2,4},{4,2},{6,0},{8,14},{10,12},{12,10},{14,8},{16,22},{18,... | collective-permute-start | bytes 393224 | tf_op jit(solution)/shard_map/cond/branch_1_fun/ppermute | solution.py:33
  167.4 11.9 %copy-start.30 = (bf16[64,1024]{1,0:T(8,128)(2,1)}, bf16[64,1024]{1,0:T(8,128)(2,1)S(1)}, u32[]{:S(2)}) copy-start(bf16[64,1024]{1,0:T(8,128)(2,1)S(1)} %collective-permute-done.7.first_ref) | copy-start | bytes 393220 | tf_op jit(solution)/shard_map/cond
  167.4 43.9 %collective-permute-start.17 = (f32[256,512]{1,0:T(8,128)S(1)}, f32[256,512]{1,0:T(8,128)S(1)}, u32[]{:S(2)}, u32[]{:S(2)}) collective-permute-start(f32[256,512]{1,0:T(8,128)S(1)} %slice_select_fusion), channel_id=1, source_target_pairs={{0,1},{1,0},{2,3},{3,2},{4,5},{5,4},{6,7},{7,6},{8,9},{9,8},{10,11... | collective-permute-start | bytes 1572872 | tf_op jit(solution)/shard_map/cond/branch_1_fun/ppermute | solution.py:33
  174.4 4.9 %copy-start.31 = (bf16[64,1024]{1,0:T(8,128)(2,1)}, bf16[64,1024]{1,0:T(8,128)(2,1)S(1)}, u32[]{:S(2)}) copy-start(bf16[64,1024]{1,0:T(8,128)(2,1)S(1)} %collective-permute-done.8.second_ref) | copy-start | bytes 393220 | tf_op jit(solution)/shard_map/cond
  179.9 31.4 %copy-start.7 = (bf16[256,512]{1,0:T(8,128)(2,1)S(1)}, bf16[256,512]{1,0:T(8,128)(2,1)}, u32[]{:S(2)}) copy-start(bf16[256,512]{1,0:T(8,128)(2,1)} %get-tuple-element.108) | copy-start | bytes 786436 | tf_op jit(solution)/shard_map/cond
  179.9 31.4 %copy-start.12 = (f32[256,512]{1,0:T(8,128)S(1)}, f32[256,512]{1,0:T(8,128)}, u32[]{:S(2)}) copy-start(f32[256,512]{1,0:T(8,128)} %copy-done.11) | copy-start | bytes 1572868 | tf_op jit(solution)/shard_map/cond
  179.9 31.4 %copy-start.18 = (bf16[256,512]{1,0:T(8,128)(2,1)S(1)}, bf16[256,512]{1,0:T(8,128)(2,1)}, u32[]{:S(2)}) copy-start(bf16[256,512]{1,0:T(8,128)(2,1)} %get-tuple-element.109) | copy-start | bytes 786436 | tf_op jit(solution)/shard_map/cond
  184.6 13.8 %collective-permute-start.11 = (bf16[80,1024]{1,0:T(8,128)(2,1)S(1)}, bf16[80,1024]{1,0:T(8,128)(2,1)S(1)}, u32[]{:S(2)}, u32[]{:S(2)}) collective-permute-start(bf16[80,1024]{1,0:T(8,128)(2,1)S(1)} %get-tuple-element.231), channel_id=1, source_target_pairs={{0,8},{2,10},{4,12},{6,14},{8,0},{10,2},{12,4},{14,6},{16,24},{18,... | collective-permute-start | bytes 491528 | tf_op jit(solution)/shard_map/cond/branch_1_fun/ppermute | solution.py:33
  186.2 12.3 %collective-permute-start.12 = (bf16[80,1024]{1,0:T(8,128)(2,1)S(1)}, bf16[80,1024]{1,0:T(8,128)(2,1)S(1)}, u32[]{:S(2)}, u32[]{:S(2)}) collective-permute-start(bf16[80,1024]{1,0:T(8,128)(2,1)S(1)} %get-tuple-element.233), channel_id=1, source_target_pairs={{0,16},{2,18},{4,20},{6,22},{8,24},{10,26},{12,28},{14,30},{16,0},... | collective-permute-start | bytes 491528 | tf_op jit(solution)/shard_map/cond/branch_1_fun/ppermute | solution.py:33
  188.5 18.1 %collective-permute-start.13 = (bf16[80,1024]{1,0:T(8,128)(2,1)S(1)}, bf16[80,1024]{1,0:T(8,128)(2,1)S(1)}, u32[]{:S(2)}, u32[]{:S(2)}) collective-permute-start(bf16[80,1024]{1,0:T(8,128)(2,1)S(1)} %get-tuple-element.232), channel_id=1, source_target_pairs={{0,24},{2,26},{4,28},{6,30},{8,16},{10,18},{12,20},{14,22},{16,8},... | collective-permute-start | bytes 491528 | tf_op jit(solution)/shard_map/cond/branch_1_fun/ppermute | solution.py:33
  207.6 8.3 %collective-permute-start.16 = (bf16[80,1024]{1,0:T(8,128)(2,1)S(1)}, bf16[80,1024]{1,0:T(8,128)(2,1)S(1)}, u32[]{:S(2)}, u32[]{:S(2)}) collective-permute-start(bf16[80,1024]{1,0:T(8,128)(2,1)S(1)} %add_convert_fusion), channel_id=1, source_target_pairs={{0,8},{2,10},{4,12},{6,14},{8,0},{10,2},{12,4},{14,6},{16,24},{18,... | collective-permute-start | bytes 491528 | tf_op jit(solution)/shard_map/cond/branch_1_fun/ppermute | solution.py:33
  212.4 9.0 %collective-permute-start.14 = (bf16[80,1024]{1,0:T(8,128)(2,1)S(1)}, bf16[80,1024]{1,0:T(8,128)(2,1)S(1)}, u32[]{:S(2)}, u32[]{:S(2)}) collective-permute-start(bf16[80,1024]{1,0:T(8,128)(2,1)S(1)} %add_convert_fusion), channel_id=1, source_target_pairs={{0,24},{2,26},{4,28},{6,30},{8,16},{10,18},{12,20},{14,22},{16,8},... | collective-permute-start | bytes 491528 | tf_op jit(solution)/shard_map/cond/branch_1_fun/ppermute | solution.py:33
  213.8 14.6 %collective-permute-start.15 = (bf16[80,1024]{1,0:T(8,128)(2,1)S(1)}, bf16[80,1024]{1,0:T(8,128)(2,1)S(1)}, u32[]{:S(2)}, u32[]{:S(2)}) collective-permute-start(bf16[80,1024]{1,0:T(8,128)(2,1)S(1)} %add_convert_fusion), channel_id=1, source_target_pairs={{0,16},{2,18},{4,20},{6,22},{8,24},{10,26},{12,28},{14,30},{16,0},... | collective-permute-start | bytes 491528 | tf_op jit(solution)/shard_map/cond/branch_1_fun/ppermute | solution.py:33
  229.5 15.9 %collective-permute-start.30 = (bf16[320,1024]{1,0:T(8,128)(2,1)}, bf16[320,1024]{1,0:T(8,128)(2,1)S(1)}, u32[]{:S(2)}, u32[]{:S(2)}) collective-permute-start(bf16[320,1024]{1,0:T(8,128)(2,1)} %get-tuple-element.175.inner_ref), channel_id=1, source_target_pairs={{0,4},{2,6},{4,0},{6,2},{8,12},{10,14},{12,8},{14,10},{16,20},{18,... | collective-permute-start | bytes 1966088 | tf_op jit(solution)/shard_map/ppermute | solution.py:33
  229.7 22.8 %collective-permute-start.32 = (bf16[320,1024]{1,0:T(8,128)(2,1)}, bf16[320,1024]{1,0:T(8,128)(2,1)S(1)}, u32[]{:S(2)}, u32[]{:S(2)}) collective-permute-start(bf16[320,1024]{1,0:T(8,128)(2,1)} %get-tuple-element.175.inner_ref), channel_id=1, source_target_pairs={{0,2},{2,0},{4,6},{6,4},{8,10},{10,8},{12,14},{14,12},{16,18},{18,... | collective-permute-start | bytes 1966088 | tf_op jit(solution)/shard_map/ppermute | solution.py:33
  245.5 4.3 %copy-start.24 = (bf16[320,1024]{1,0:T(8,128)(2,1)}, bf16[320,1024]{1,0:T(8,128)(2,1)S(1)}, u32[]{:S(2)}) copy-start(bf16[320,1024]{1,0:T(8,128)(2,1)S(1)} %collective-permute-done.30.inner_ref) | copy-start | bytes 1966084
  245.5 13.1 %collective-permute-start.31 = (bf16[320,1024]{1,0:T(8,128)(2,1)S(1)}, bf16[320,1024]{1,0:T(8,128)(2,1)S(1)}, u32[]{:S(2)}, u32[]{:S(2)}) collective-permute-start(bf16[320,1024]{1,0:T(8,128)(2,1)S(1)} %collective-permute-done.30.inner_ref), channel_id=1, source_target_pairs={{0,2},{2,0},{4,6},{6,4},{8,10},{10,8},{12,14},{14,12},{16,18},{18,... | collective-permute-start | bytes 1966088 | tf_op jit(solution)/shard_map/ppermute | solution.py:33
  (16 other events, 16.7 us)
Sparse Core Ops, SparseCore 0:
  81.7 120.9 all-reduce.2

commit v9 on v8

--- a/solution.py
+++ b/solution.py
@@ -644,13 +644,9 @@
     inner_ref,
     conv_weight_ref,
     mask_ref,
-    wait_ref,
-    inner_grad_ref,
-    edge_ref,
-    small_ref,
-    inner,
-    shifted,
+    *rest,
 ):
+    inner_grad_ref, edge_ref, small_ref, inner, shifted = rest[-5:]
     rows = act_ref.shape[0]
     taps = conv_weight_ref.shape[0]
     columns = select_ref.shape[0]
@@ -689,7 +685,7 @@
 
 
 def convolve_grad(
-    select_grad, other, select_weight, act_grad, convolved, act, projected, conv_weight, masks, wait
+    select_grad, other, select_weight, act_grad, convolved, act, projected, conv_weight, masks, waits
 ):
     rows, width = act.shape
     extended = rows + halo
@@ -710,8 +706,8 @@
             part_spec(0, extended),
             column_spec(taps),
             whole_spec(rows, masks.shape[1]),
-            pl.BlockSpec(memory_space=pl.ANY),
-        ],
+        ]
+        + [pl.BlockSpec(memory_space=pl.ANY)] * len(waits),
         [column_spec(rows), column_spec(16), column_spec(small)],
         [
             jax.ShapeDtypeStruct((rows, width), bf16),
@@ -728,7 +724,7 @@
         projected,
         conv_weight,
         masks,
-        wait,
+        *waits,
     )
 
 
@@ -821,7 +817,8 @@
     )(ids, tokens)
 
 
-def small_kernel(place_ref, scan_ref, conv_ref, gain_ref, other_gain_ref, keep_ref, sends_ref, rows):
+def small_kernel(place_ref, scan_ref, conv_ref, gain_ref, other_gain_ref, keep_ref, *rest):
+    sends_refs, rows = rest[:3], rest[3]
     at = 0
     for ref in (scan_ref, conv_ref):
         rows[at : at + ref.shape[0], :] = ref[...]
@@ -836,7 +833,7 @@
         if n == 0:
             keep_ref[...] = block
         else:
-            sends_ref[n - 1] = block.astype(bf16)
+            sends_refs[n - 1][...] = block.astype(bf16)
 
 
 def small_quarters(place, scan_small, conv_small, gain, other_gain):
@@ -846,10 +843,8 @@
         small_kernel,
         in_specs=[pl.BlockSpec(memory_space=pltpu.SMEM)]
         + [pl.BlockSpec(memory_space=pltpu.VMEM)] * 4,
-        out_shape=[
-            jax.ShapeDtypeStruct((rows // 4, width), f32),
-            jax.ShapeDtypeStruct((3, rows // 4, width), bf16),
-        ],
+        out_shape=[jax.ShapeDtypeStruct((rows // 4, width), f32)]
+        + [jax.ShapeDtypeStruct((rows // 4, width), bf16)] * 3,
         scratch_shapes=[pltpu.VMEM((rows, width), f32)],
         cost_estimate=tiny_cost,
         name="small_quarters",
@@ -869,7 +864,7 @@
     third_ref,
     *rest,
 ):
-    keep_ref, sends_ref, piece, small = rest[-4:]
+    keep_ref, *sends_refs, piece, small = rest[-6:]
     total = None
     for n, grads in enumerate((own_ref, near_ref, far_ref, last_ref)):
         part = lax.dot_general(normed_ref[n], grads[...], contract_first, preferred_element_type=f32)
@@ -887,8 +882,8 @@
             keep_ref[:rows, :] = inner_rows
             keep_ref[rows:, :] = small_rows
         else:
-            sends_ref[n - 1, :rows, :] = inner_rows.astype(bf16)
-            sends_ref[n - 1, rows:, :] = small_rows.astype(bf16)
+            sends_refs[n - 1][:rows, :] = inner_rows.astype(bf16)
+            sends_refs[n - 1][rows:, :] = small_rows.astype(bf16)
 
 
 def inner_quarter(place, own, near, far, last, normed, smalls, waits):
@@ -901,10 +896,8 @@
         in_specs=[pl.BlockSpec(memory_space=pltpu.SMEM)]
         + [pl.BlockSpec(memory_space=pltpu.VMEM)] * 9
         + [pl.BlockSpec(memory_space=pl.ANY)] * len(waits),
-        out_shape=[
-            jax.ShapeDtypeStruct((rows, width), f32),
-            jax.ShapeDtypeStruct((3, rows, width), bf16),
-        ],
+        out_shape=[jax.ShapeDtypeStruct((rows, width), f32)]
+        + [jax.ShapeDtypeStruct((rows, width), bf16)] * 3,
         scratch_shapes=[pltpu.VMEM((quarter, width), f32), pltpu.VMEM((spare, width), f32)],
         compiler_params=pltpu.CompilerParams(vmem_limit_bytes=vmem_bytes),
         cost_estimate=tiny_cost,
@@ -975,7 +968,7 @@
     return jnp.exp(decay * total)
 
 
-def round_kernel(second_ref, decay_log_ref, own_ref, other_ref, passed_ref, ends_ref, new_passed_ref):
+def round_kernel(second_ref, decay_log_ref, own_ref, other_ref, passed_ref, new_passed_ref, *ends_refs):
     count = decay_log_ref.shape[0]
     decay = -jnp.exp(decay_log_ref[...])
     second = second_ref[0] > 0
@@ -986,9 +979,15 @@
     own, other = split(own_ref), split(other_ref)
     early = [jnp.where(second, b, a) for a, b in zip(own, other)]
     late = [jnp.where(second, a, b) for a, b in zip(own, other)]
-    ends_ref[:count, :] = late[0] + through(decay, late[2]) * early[0]
-    ends_ref[count : 2 * count, :] = early[1] + through(decay, early[2]) * late[1]
-    ends_ref[2 * count :, :] = jnp.broadcast_to(early[2] + late[2], (8, decay.shape[1]))
+    state = late[0] + through(decay, late[2]) * early[0]
+    adjoint = early[1] + through(decay, early[2]) * late[1]
+    if len(ends_refs) == 2:
+        ends_refs[0][...] = state
+        ends_refs[1][...] = adjoint
+    else:
+        ends_refs[0][:count, :] = state
+        ends_refs[0][count : 2 * count, :] = adjoint
+        ends_refs[0][2 * count :, :] = jnp.broadcast_to(early[2] + late[2], (8, decay.shape[1]))
     before, after = passed_ref[:count], passed_ref[count : 2 * count]
     before_steps = passed_ref[2 * count : 2 * count + 1]
     after_steps = passed_ref[2 * count + 1 : 2 * count + 2]
@@ -1006,19 +1005,17 @@
     passed = jnp.zeros((2 * count + 8, width), f32)
     packed = ends
     vmem = pl.BlockSpec(memory_space=pltpu.VMEM)
-    for k in range(2):
-        packed, passed = pl.pallas_call(
+    for k, kinds in enumerate(([ends], [decay_log, decay_log])):
+        passed, *out = pl.pallas_call(
             round_kernel,
             in_specs=[pl.BlockSpec(memory_space=pltpu.SMEM)] + [vmem] * 4,
-            out_shape=[
-                jax.ShapeDtypeStruct(ends.shape, f32),
-                jax.ShapeDtypeStruct(passed.shape, f32),
-            ],
+            out_shape=[jax.ShapeDtypeStruct(kind.shape, f32) for kind in [passed] + kinds],
             cost_estimate=tiny_cost,
             name="carry_round",
         )((place >> k & 1)[None], decay_log, packed, swapped(packed, "wide", 2**k), passed)
-    from_before = passed_along(packed[:count], "wide", 4)
-    from_after = passed_along(packed[count : 2 * count], "wide", -4)
+        packed = out[0]
+    from_before = passed_along(out[0], "wide", 4)
+    from_after = passed_along(out[1], "wide", -4)
     return passed, from_before, from_after
 
 
@@ -1095,7 +1092,6 @@
     )
     gated, gate_grad = pair[0], pair[1]
     normed = normed_ext[:rows]
-    normed_four = quarter_of_four(after(normed, pair))
     products = (
         lax.dot_general(gated, cot_whole, contract_first, preferred_element_type=f32).astype(bf16),
         lax.dot_general(normed, gate_grad, contract_first, preferred_element_type=f32).astype(bf16),
@@ -1110,6 +1106,7 @@
         return jnp.where(right_half, high, low), jnp.where(right_half, low, high)
 
     def after_forward(products):
+        normed_four = quarter_of_four(normed)
         out_part = jnp.dot(gated, out_weight, preferred_element_type=f32)
         out_mine, out_other = narrow_halves(out_part)
         out_theirs = swapped(out_other, "narrow", 1)
@@ -1140,7 +1137,7 @@
             projected,
             conv_weight,
             masks,
-            out_theirs,
+            [out_theirs, normed_four],
         )
         from_next = passed_along(edges[:8], "wide", -1)
         last_rows = edges[8:] + jnp.where(same_as_last, from_next, 0.0)
@@ -1152,19 +1149,20 @@
         )
         gain_part = jnp.sum(normed_part * whole * inverse, axis=0, keepdims=True)
         row_part = jnp.sum(normed_part * norm_gain * whole, axis=1)[None]
-        keep, sends = small_quarters(
+        keep, *sends = small_quarters(
             four_place, scan_small, conv_small, gain_part, swapped(gain_part, "narrow", 1)
         )
         smalls = [keep] + [swapped(sends[n - 1], "wide", n) for n in (1, 2, 3)]
         normed_mine, normed_other = narrow_halves(normed_part)
         row_theirs = swapped(row_part, "narrow", 1)
         normed_theirs = swapped(normed_other, "narrow", 1)
-        keep, sends = inner_quarter(
+        near = after(near, *sends)
+        keep, *sends = inner_quarter(
             (wide_place >> 2 & 3)[None],
             inner_grad,
             near,
             far,
-            swapped(after(near, sends), "wide", 1),
+            swapped(near, "wide", 1),
             normed_four,
             smalls,
             [row_theirs],
@@ -1195,13 +1193,16 @@
     )
 
     out_weight_grad = out_sum.astype(f32)
-    near = swapped(held, "wide", 2)
-    quarters = (held, swapped(held, "wide", 1), near, swapped(near, "wide", 1))
+    def join(flip, quarter, *waits):
+        return joined(four_place, flip, gate_sum, quarter, results, waits)
+
     results = []
-    for flip, quarter in enumerate(quarters):
-        results = joined(
-            four_place, flip, gate_sum, quarter, results, [] if flip else [out_weight_grad]
-        )
+    results = join(0, held, out_weight_grad)
+    results = join(1, swapped(held, "wide", 1))
+    near = after(swapped(held, "wide", 2), results[1])
+    far = swapped(near, "wide", 1)
+    results = join(2, near)
+    results = join(3, far)
     in_weight_grad, small_sum = results
     conv_at = rank + count + 16
     gain_at = conv_at + columns + 16

time: 272 us -> 259 us (0.952)
  waiting for transfers between devices: 87.3 us -> 76 us
  local copies, waits for them, and re-layouts: 18.5 us -> 15.4 us
    ppermute x28, waiting for transfers between devices: 85.3 us -> 68.1 us  [swapped(): return lax.ppermute(array, axis, [(i, i ^ bit) for i in range(peers)])]
    ppermute x4, waiting for transfers between devices: 1.96 us -> 7.82 us  [passed_along(): return lax.ppermute(array, axis, pairs)]
    ppermute x4, starting transfers between devices: 7.9 us -> 11.1 us  [passed_along(): return lax.ppermute(array, axis, pairs)]
    ppermute x1, starting transfers between devices: 4.07 us -> 1.34 us  [to_next_both(): lax.ppermute(array, ('wide', 'narrow'), pairs)]
  transfers between devices with their start and end apart: 34 -> 34, of which waited for: 20 -> 17; matrix products, arithmetic and copies ran while one was open for 12% -> 13% of each run, Pallas kernels for 18% -> 19%
where the time goes in v9:
time: 259 us; the launch traced here: 257 us
  Pallas kernels  76.3 us (29%)
  waiting for transfers between devices  76 us (29%)
  starting transfers between devices  42.7 us (16%)
  other arithmetic  15.8 us (6%)
  local copies, waits for them, and re-layouts  15.4 us (6%)
  matrix products  15.3 us (6%)
  between operations  15 us (6%)
    ppermute x28, waiting for transfers between devices, swapped(): return lax.ppermute(array, axis, [(i, i ^ bit) for i in range(peers)])  68.1 us
    pallas_call x5, Pallas kernels, call(): pl.pallas_call(kernel, grid=(width // scan_width,), in_specs=in_specs, ou...  50.5 us
    ppermute x28, starting transfers between devices, swapped(): return lax.ppermute(array, axis, [(i, i ^ bit) for i in range(peers)])  30.2 us
    ppermute x4, starting transfers between devices, passed_along(): return lax.ppermute(array, axis, pairs)  11.1 us
    pallas_call x4, Pallas kernels, joined(): pl.pallas_call(join_kernel, grid_spec=pltpu.PrefetchScalarGridSpec(num_sc...  10.6 us
    ppermute x4, waiting for transfers between devices, passed_along(): return lax.ppermute(array, axis, pairs)  7.82 us
  transfers between devices with their start and end apart: 34, of which 17 were waited for; matrix products, arithmetic and copies ran while one was open for 13% of the time, Pallas kernels for 19%

profile of v9, /device:TPU:0, one launch (start us, length us, event | category | flops | bytes accessed | tf_op | source)
XLA Modules:
  0.0 256.6 jit_solution(3270148314439589407)
XLA Ops:
  7.2 3.0 %collective-permute-start.21 = (bf16[256,512]{1,0:T(8,128)(2,1)}, bf16[256,512]{1,0:T(8,128)(2,1)S(1)}, u32[]{:S(2)}, u32[]{:S(2)}) collective-permute-start(bf16[256,512]{1,0:T(8,128)(2,1)} %own_ref.1), channel_id=1, source_target_pairs={{0,1},{1,0},{2,3},{3,2},{4,5},{5,4},{6,7},{7,6},{8,9},{9,8},{10,11... | collective-permute-start | bytes 786440 | tf_op jit(solution)/shard_map/ppermute | solution.py:33
  10.3 1.4 edge_rows.1
  11.6 1.3 collective-permute-start.23
  13.0 4.0 %collective-permute-start.22 = (bf16[16,512]{1,0:T(8,128)(2,1)}, bf16[16,512]{1,0:T(8,128)(2,1)S(1)}, u32[]{:S(2)}, u32[]{:S(2)}) collective-permute-start(bf16[16,512]{1,0:T(8,128)(2,1)} %edge_rows.1), channel_id=1, source_target_pairs={{0,2},{2,4},{4,6},{6,8},{8,10},{10,12},{12,14},{14,16},{16,18},{18... | collective-permute-start | bytes 49160 | tf_op jit(solution)/shard_map/ppermute | solution.py:28
  17.0 1.6 collective-permute-start.25
  19.3 2.4 normalized.1
  21.7 4.0 %fusion.20.inner_ref.gate_ref = bf16[2,272,1024]{2,1,0:T(8,128)(2,1)S(1)} fusion(bf16[1024,2,1024]{2,1,0:T(2,128)(2,1)} %param.17, bf16[272,1024]{1,0:T(8,128)(2,1)} %get-tuple-element.162), kind=kOutput, calls=%fused_computation.45 | convolution fusion | flops 1141407744 | bytes 5865472 | tf_op jit(solution)/shard_map/td,dce->cte/dot_general | solution.py:1057
  25.7 3.1 %convolve.1 = (f32[256,1024]{1,0:T(8,128)}, bf16[256,1024]{1,0:T(8,128)(2,1)S(1)}, f32[96,256]{1,0:T(8,128)S(1)}) custom-call(bf16[2,272,1024]{2,1,0:T(8,128)(2,1)S(1)} %fusion.20.inner_ref.gate_ref, f32[4,1024]{1,0:T(4,128)S(1)} %copy-done.30, f32[1,1024]{1,0:T(1,128)} %bitcast.52, bf16[96,1024]{1,0:T(8,128)(2,1)S(1)} %copy-done.15, ...), custom_call_target="tpu_custom_call" | custom-call | flops 1 | bytes 1 | tf_op jit(solution)/shard_map/convolve/pallas_call | solution.py:129
  30.6 2.8 %collective-permute-done.24.other_ref = f32[96,256]{1,0:T(8,128)S(1)} collective-permute-done((f32[96,256]{1,0:T(8,128)S(1)}, f32[96,256]{1,0:T(8,128)S(1)}, u32[]{:S(2)}, u32[]{:S(2)}) %collective-permute-start.24) | collective-permute-done | bytes 98336 | tf_op jit(solution)/shard_map/ppermute | solution.py:33
  34.1 9.9 %scan_ends.1 = (f32[256,1024]{1,0:T(8,128)}, f32[256,1024]{1,0:T(8,128)}, f32[40,1024]{1,0:T(8,128)}) custom-call(f32[96,256]{1,0:T(8,128)S(1)} %get-tuple-element.164.selected_ref, f32[96,256]{1,0:T(8,128)S(1)} %collective-permute-done.24.other_ref, bf16[64,1024]{1,0:T(8,128)(2,1)S(1)} %copy-done.19, f32[1,1024]{1,0:T(1,128)} %bitcast.53, ...), custom_call_target="tpu_custom_call" | custom-call | flops 1 | bytes 1 | tf_op jit(solution)/shard_map/scan_ends/pallas_call | solution.py:129
  44.0 1.7 collective-permute-done.26.other_ref
  46.5 1.8 carry_round.2
  48.3 1.7 collective-permute-start.27
  50.0 4.9 %collective-permute-done.27.other_ref = f32[40,1024]{1,0:T(8,128)} collective-permute-done((f32[40,1024]{1,0:T(8,128)}, f32[40,1024]{1,0:T(8,128)}, u32[]{:S(2)}, u32[]{:S(2)}) %collective-permute-start.27) | collective-permute-done | bytes 163872 | tf_op jit(solution)/shard_map/ppermute | solution.py:33
  54.9 1.8 carry_round.3
  56.7 4.6 %collective-permute-start.28 = (f32[16,1024]{1,0:T(8,128)}, f32[16,1024]{1,0:T(8,128)S(1)}, u32[]{:S(2)}, u32[]{:S(2)}) collective-permute-start(f32[16,1024]{1,0:T(8,128)} %get-tuple-element.172), channel_id=1, source_target_pairs={{0,8},{2,10},{4,12},{6,14},{8,16},{10,18},{12,20},{14,22},{16,24},... | collective-permute-start | bytes 196616 | tf_op jit(solution)/shard_map/ppermute | solution.py:28
  61.3 2.2 collective-permute-done.28.entering_ref
  64.1 9.8 %scan_forward.1 = (bf16[2,256,1024]{2,1,0:T(8,128)(2,1)}, f32[16,1024]{1,0:T(8,128)}) custom-call(f32[96,256]{1,0:T(8,128)S(1)} %get-tuple-element.164.selected_ref, f32[96,256]{1,0:T(8,128)} %copy-done.14, f32[256,1024]{1,0:T(8,128)} %get-tuple-element.167.step_ref, bf16[256,1024]{1,0:T(8,128)(2,1)S(1)} %get-tuple-element.165.act_ref, ...), custom_call_target="tpu_custom_call" | custom-call | flops 1 | bytes 1 | tf_op jit(solution)/shard_map/scan_forward/pallas_call | solution.py:129
  73.9 3.2 %convolution_convert_fusion.1 = bf16[1024,1024]{1,0:T(8,128)(2,1)} fusion(bf16[2,256,1024]{2,1,0:T(8,128)(2,1)} %get-tuple-element.175, bf16[272,1024]{1,0:T(8,128)(2,1)S(1)} %copy-done.9), kind=kOutput, calls=%fused_computation.43 | convolution fusion | flops 537919488 | bytes 3145728 | tf_op jit(solution)/shard_map/dot_general | solution.py:1097
  77.1 2.1 convolution_convert_fusion
  81.1 1.9 slice.52
  83.0 2.3 slice_convert_fusion
  85.3 1.3 collective-permute-start.29
  87.4 5.6 %collective-permute-done.29 = f32[16,1024]{1,0:T(8,128)S(1)} collective-permute-done((f32[16,1024]{1,0:T(8,128)S(1)}, f32[16,1024]{1,0:T(8,128)S(1)}, u32[]{:S(2)}, u32[]{:S(2)}) %collective-permute-start.29) | collective-permute-done | bytes 65568 | tf_op jit(solution)/shard_map/ppermute | solution.py:28
  93.0 130.3 %conditional.1 = (bf16[320,1024]{1,0:T(8,128)(2,1)}, bf16[256,512]{1,0:T(8,128)(2,1)}, bf16[256,512]{1,0:T(8,128)(2,1)}) conditional(s32[]{:T(128)} %bitcast.14, () %tuple.16, (s32[]{:T(128)}, f32[1024]{0:T(1024)S(1)}, f32[96,256]{1,0:T(8,128)S(1)}, f32[96,256]{1,0:T(8,128)}, f32[256,1024]{1,0:T(8,128)}, /*index=5*/f32[256,1024]{1,0:T(8,128)}, ...), branch_computations={%region_0.1_spmd, %region_1.4_spmd} | conditional | flops 1620648192 | bytes 62924520 | solution.py:1188
  95.5 1.5 collective-permute-start.1
  96.9 1.1 dynamic-slice_bitcast_fusion
  98.8 1.2 collective-permute-start.4
  100.0 23.7 %scan_backward.1 = (f32[256,1024]{1,0:T(8,128)}, f32[96,256]{1,0:T(8,128)}, f32[96,1024]{1,0:T(8,128)}) custom-call(f32[96,256]{1,0:T(8,128)S(1)} %get-tuple-element.70.selected_ref, f32[96,256]{1,0:T(8,128)} %get-tuple-element.71.other_ref, f32[256,1024]{1,0:T(8,128)} %get-tuple-element.72.step_pre_ref, f32[256,1024]{1,0:T(8,128)} %get-tuple-element.73.step_ref, ...), custom_call_target="tpu_custom_call" | custom-call | flops 1 | bytes 1 | tf_op jit(solution)/shard_map/cond/branch_1_fun/scan_backward/pallas_call | solution.py:129
  125.8 3.2 %collective-permute-done.other_ref = f32[96,256]{1,0:T(8,128)S(1)} collective-permute-done((f32[96,256]{1,0:T(8,128)}, f32[96,256]{1,0:T(8,128)S(1)}, u32[]{:S(2)}, u32[]{:S(2)}) %collective-permute-start) | collective-permute-done | bytes 98336 | tf_op jit(solution)/shard_map/cond/branch_1_fun/ppermute | solution.py:33
  129.6 4.0 %convolve_grad.1 = (bf16[256,1024]{1,0:T(8,128)(2,1)}, f32[16,1024]{1,0:T(8,128)}, f32[112,1024]{1,0:T(8,128)}) custom-call(f32[96,256]{1,0:T(8,128)} %get-tuple-element.84.select_grad_ref, f32[96,256]{1,0:T(8,128)} %copy-done.27, bf16[96,1024]{1,0:T(8,128)(2,1)S(1)} %copy-done.16, f32[256,1024]{1,0:T(8,128)} %get-tuple-element.86.act_grad_ref, ...), custom_call_target="tpu_custom_call" | custom-call | flops 1 | bytes 1 | tf_op jit(solution)/shard_map/cond/branch_1_fun/convolve_grad/pallas_call | solution.py:129
  134.4 1.3 collective-permute-start.5
  136.5 1.1 slice.36
  138.6 2.0 collective-permute-start.6
  140.5 4.6 %multiply_reduce_fusion = (f32[256]{0:T(256)S(1)}, f32[1024]{0:T(1024)S(1)}, f32[256,1024]{1,0:T(8,128)S(1)}) fusion(f32[256,1024]{1,0:T(8,128)} %get-tuple-element.101, f32[1024]{0:T(1024)S(1)} %get-tuple-element.107, f32[256]{0:T(256)S(1)} %bitcast.50, bf16[1024,2,1024]{2,1,0:T(2,128)(2,1)} %get-tuple-element.222, ...), kind=kOutput, calls=%fused_computation.6 | convolution fusion | flops 1075837696 | bytes 7350272 | tf_op jit(solution)/shard_map/cond/branch_1_fun/cte,dce->td/dot_general | solution.py:1147
  145.6 1.6 collective-permute-start.8
  147.2 1.6 collective-permute-done.7.other_gain_ref
  149.4 2.0 small_quarters.1
  151.4 4.6 %collective-permute-done.6.refs_0_ = bf16[256,1024]{1,0:T(8,128)(2,1)} collective-permute-done((bf16[256,1024]{1,0:T(8,128)(2,1)S(1)}, bf16[256,1024]{1,0:T(8,128)(2,1)}, u32[]{:S(2)}, u32[]{:S(2)}) %collective-permute-start.6) | collective-permute-done | bytes 524320 | tf_op jit(solution)/shard_map/cond/branch_1_fun/ppermute | solution.py:33
  156.0 1.3 collective-permute-start.9
  158.8 1.5 collective-permute-start.20
  160.9 2.1 collective-permute-start.11
  163.1 5.5 %collective-permute-done.11.second_ref = bf16[64,1024]{1,0:T(8,128)(2,1)S(1)} collective-permute-done((bf16[64,1024]{1,0:T(8,128)(2,1)S(1)}, bf16[64,1024]{1,0:T(8,128)(2,1)S(1)}, u32[]{:S(2)}, u32[]{:S(2)}) %collective-permute-start.11) | collective-permute-done | bytes 131104 | tf_op jit(solution)/shard_map/cond/branch_1_fun/ppermute | solution.py:33
  168.6 4.2 %collective-permute-done.12.third_ref = bf16[64,1024]{1,0:T(8,128)(2,1)S(1)} collective-permute-done((bf16[64,1024]{1,0:T(8,128)(2,1)S(1)}, bf16[64,1024]{1,0:T(8,128)(2,1)S(1)}, u32[]{:S(2)}, u32[]{:S(2)}) %collective-permute-start.12) | collective-permute-done | bytes 131104 | tf_op jit(solution)/shard_map/cond/branch_1_fun/ppermute | solution.py:33
  173.5 3.6 %inner_quarter.1 = (f32[80,1024]{1,0:T(8,128)}, bf16[80,1024]{1,0:T(8,128)(2,1)}, bf16[80,1024]{1,0:T(8,128)(2,1)}, bf16[80,1024]{1,0:T(8,128)(2,1)}) custom-call(s32[1]{0:T(128)} %bitcast.place_ref, bf16[256,1024]{1,0:T(8,128)(2,1)} %copy-done.8, bf16[256,1024]{1,0:T(8,128)(2,1)} %after.2.near_ref, bf16[256,1024]{1,0:T(8,128)(2,1)} %collective-permute-done.8.far_ref, ...), custom_call_target="tpu_custom_call" | custom-call | flops 1 | bytes 1 | tf_op jit(solution)/shard_map/cond/branch_1_fun/inner_quarter/pallas_call | solution.py:894
  177.1 1.3 collective-permute-start.14
  178.4 1.7 collective-permute-start.15
  180.1 1.4 collective-permute-start.16
  182.2 8.9 %collective-permute-done.14 = bf16[80,1024]{1,0:T(8,128)(2,1)S(1)} collective-permute-done((bf16[80,1024]{1,0:T(8,128)(2,1)}, bf16[80,1024]{1,0:T(8,128)(2,1)S(1)}, u32[]{:S(2)}, u32[]{:S(2)}) %collective-permute-start.14) | collective-permute-done | bytes 163872 | tf_op jit(solution)/shard_map/cond/branch_1_fun/ppermute | solution.py:33
  192.0 11.0 %collective-permute-done.16 = bf16[80,1024]{1,0:T(8,128)(2,1)S(1)} collective-permute-done((bf16[80,1024]{1,0:T(8,128)(2,1)}, bf16[80,1024]{1,0:T(8,128)(2,1)S(1)}, u32[]{:S(2)}, u32[]{:S(2)}) %collective-permute-start.16) | collective-permute-done | bytes 163872 | tf_op jit(solution)/shard_map/cond/branch_1_fun/ppermute | solution.py:33
  203.0 1.1 add_convert_fusion
  204.1 1.7 collective-permute-start.19
  205.7 2.2 fusion.12
  208.0 1.2 collective-permute-start.18
  209.2 1.6 collective-permute-start.17
  210.7 4.5 %collective-permute-done.19 = bf16[80,1024]{1,0:T(8,128)(2,1)S(1)} collective-permute-done((bf16[80,1024]{1,0:T(8,128)(2,1)S(1)}, bf16[80,1024]{1,0:T(8,128)(2,1)S(1)}, u32[]{:S(2)}, u32[]{:S(2)}) %collective-permute-start.19) | collective-permute-done | bytes 163872 | tf_op jit(solution)/shard_map/cond/branch_1_fun/ppermute | solution.py:33
  215.3 6.9 %collective-permute-done.18 = bf16[80,1024]{1,0:T(8,128)(2,1)S(1)} collective-permute-done((bf16[80,1024]{1,0:T(8,128)(2,1)S(1)}, bf16[80,1024]{1,0:T(8,128)(2,1)S(1)}, u32[]{:S(2)}, u32[]{:S(2)}) %collective-permute-start.18) | collective-permute-done | bytes 163872 | tf_op jit(solution)/shard_map/cond/branch_1_fun/ppermute | solution.py:33
  223.9 4.1 %convert_element_type.58.rest_0_ = f32[1024,1024]{1,0:T(8,128)} convert(bf16[1024,1024]{1,0:T(8,128)(2,1)} %get-tuple-element.232) | non-fusion elementwise | flops 1048576 | bytes 6291456 | tf_op jit(solution)/shard_map/convert_element_type | solution.py:1195
  227.9 2.6 %joined.4 = (f32[1024,2,1024]{2,1,0:T(2,128)}, f32[256,1024]{1,0:T(8,128)}) custom-call(s32[1]{0:T(128)} %bitcast.25.place_ref, bf16[1024,1024]{1,0:T(8,128)(2,1)} %get-tuple-element.231.gate_ref, bf16[320,1024]{1,0:T(8,128)(2,1)} %get-tuple-element.181.inner_ref, f32[1024,1024]{1,0:T(8,128)} %convert_element_type.58.rest_0_), custom_call_target="tpu_custom_call" | custom-call | flops 1 | bytes 1 | tf_op jit(solution)/shard_map/joined/pallas_call | solution.py:924
  231.4 2.7 %joined.5 = (f32[1024,2,1024]{2,1,0:T(2,128)}, f32[256,1024]{1,0:T(8,128)}) custom-call(s32[1]{0:T(128)} %bitcast.25.place_ref, bf16[1024,1024]{1,0:T(8,128)(2,1)} %get-tuple-element.231.gate_ref, bf16[320,1024]{1,0:T(8,128)(2,1)} %copy-done.17, f32[1024,2,1024]{2,1,0:T(2,128)} %get-tuple-element.182.rest_0_, ...), custom_call_target="tpu_custom_call", output_to_operand_aliasing={{0}: (3, {}), {1}: (4, {})} | custom-call | flops 1 | bytes 1 | tf_op jit(solution)/shard_map/joined/pallas_call | solution.py:924
  234.1 6.6 %collective-permute-done.30.refs_0_ = bf16[320,1024]{1,0:T(8,128)(2,1)S(1)} collective-permute-done((bf16[320,1024]{1,0:T(8,128)(2,1)}, bf16[320,1024]{1,0:T(8,128)(2,1)S(1)}, u32[]{:S(2)}, u32[]{:S(2)}) %collective-permute-start.30) | collective-permute-done | bytes 655392 | tf_op jit(solution)/shard_map/ppermute | solution.py:33
  241.5 2.7 %joined.6 = (f32[1024,2,1024]{2,1,0:T(2,128)}, f32[256,1024]{1,0:T(8,128)}) custom-call(s32[1]{0:T(128)} %bitcast.25.place_ref, bf16[1024,1024]{1,0:T(8,128)(2,1)} %get-tuple-element.231.gate_ref, bf16[320,1024]{1,0:T(8,128)(2,1)} %after.3.inner_ref, f32[1024,2,1024]{2,1,0:T(2,128)} %get-tuple-element.185.rest_0_, ...), custom_call_target="tpu_custom_call", output_to_operand_aliasing={{0}: (3, {}), {1}: (4, {})} | custom-call | flops 1 | bytes 1 | tf_op jit(solution)/shard_map/joined/pallas_call | solution.py:924
  245.0 2.7 %joined.7 = (f32[1024,2,1024]{2,1,0:T(2,128)}, f32[256,1024]{1,0:T(8,128)}) custom-call(s32[1]{0:T(128)} %bitcast.25.place_ref, bf16[1024,1024]{1,0:T(8,128)(2,1)} %get-tuple-element.231.gate_ref, bf16[320,1024]{1,0:T(8,128)(2,1)} %copy-done.18, f32[1024,2,1024]{2,1,0:T(2,128)} %get-tuple-element.186.rest_0_, ...), custom_call_target="tpu_custom_call", output_to_operand_aliasing={{0}: (3, {}), {1}: (4, {})} | custom-call | flops 1 | bytes 1 | tf_op jit(solution)/shard_map/joined/pallas_call | solution.py:924
  247.7 2.1 small_parts.1
  (137 shorter events, 24.5 us)
Async XLA Ops:
  7.2 216.7 %all-reduce.3.cloned.1.call-start = ((), (), s32[]{:S(2)}) async-start(), calls=%async_computation | async-start | bytes 8388608 | tf_op jit(solution)/shard_map/psum | solution.py:1099
  7.2 11.4 %collective-permute-start.21 = (bf16[256,512]{1,0:T(8,128)(2,1)}, bf16[256,512]{1,0:T(8,128)(2,1)S(1)}, u32[]{:S(2)}, u32[]{:S(2)}) collective-permute-start(bf16[256,512]{1,0:T(8,128)(2,1)} %own_ref.1), channel_id=1, source_target_pairs={{0,1},{1,0},{2,3},{3,2},{4,5},{5,4},{6,7},{7,6},{8,9},{9,8},{10,11... | collective-permute-start | bytes 786440 | tf_op jit(solution)/shard_map/ppermute | solution.py:33
  11.6 7.0 %collective-permute-start.23 = (bf16[16,512]{1,0:T(8,128)(2,1)}, bf16[16,512]{1,0:T(8,128)(2,1)S(1)}, u32[]{:S(2)}, u32[]{:S(2)}) collective-permute-start(bf16[16,512]{1,0:T(8,128)(2,1)} %edge_rows.1), channel_id=1, source_target_pairs={{0,3},{1,2},{2,5},{3,4},{4,7},{5,6},{6,9},{7,8},{8,11},{9,10},{10,... | collective-permute-start | bytes 49160 | tf_op jit(solution)/shard_map/ppermute | solution.py:51
  13.0 5.6 %collective-permute-start.22 = (bf16[16,512]{1,0:T(8,128)(2,1)}, bf16[16,512]{1,0:T(8,128)(2,1)S(1)}, u32[]{:S(2)}, u32[]{:S(2)}) collective-permute-start(bf16[16,512]{1,0:T(8,128)(2,1)} %edge_rows.1), channel_id=1, source_target_pairs={{0,2},{2,4},{4,6},{6,8},{8,10},{10,12},{12,14},{14,16},{16,18},{18... | collective-permute-start | bytes 49160 | tf_op jit(solution)/shard_map/ppermute | solution.py:28
  17.0 12.8 %collective-permute-start.25 = (bf16[256,512]{1,0:T(8,128)(2,1)}, bf16[256,512]{1,0:T(8,128)(2,1)S(1)}, u32[]{:S(2)}, u32[]{:S(2)}) collective-permute-start(bf16[256,512]{1,0:T(8,128)(2,1)} %param.27), channel_id=1, source_target_pairs={{0,1},{1,0},{2,3},{3,2},{4,5},{5,4},{6,7},{7,6},{8,9},{9,8},{10,11... | collective-permute-start | bytes 786440 | tf_op jit(solution)/shard_map/ppermute | solution.py:33
  21.7 4.0 %copy-start.15 = (bf16[96,1024]{1,0:T(8,128)(2,1)S(1)}, bf16[96,1024]{1,0:T(8,128)(2,1)}, u32[]{:S(2)}) copy-start(bf16[96,1024]{1,0:T(8,128)(2,1)} %select_ref.1) | copy-start | bytes 589828
  21.7 4.0 %copy-start.30 = (f32[4,1024]{1,0:T(4,128)S(1)}, f32[4,1024]{1,0:T(4,128)}, u32[]{:S(2)}) copy-start(f32[4,1024]{1,0:T(4,128)} %conv_weight_ref.1) | copy-start | bytes 49156
  21.7 8.1 %copy-start.11 = (bf16[256,512]{1,0:T(8,128)(2,1)S(1)}, bf16[256,512]{1,0:T(8,128)(2,1)}, u32[]{:S(2)}) copy-start(bf16[256,512]{1,0:T(8,128)(2,1)} %param.27) | copy-start | bytes 786436
  25.7 4.2 %copy-start = (bf16[1024,1024]{1,0:T(8,128)(2,1)S(1)}, bf16[1024,1024]{1,0:T(8,128)(2,1)}, u32[]{:S(2)}) copy-start(bf16[1024,1024]{1,0:T(8,128)(2,1)} %param.25) | copy-start | bytes 6291460
  28.9 4.6 %collective-permute-start.24 = (f32[96,256]{1,0:T(8,128)S(1)}, f32[96,256]{1,0:T(8,128)S(1)}, u32[]{:S(2)}, u32[]{:S(2)}) collective-permute-start(f32[96,256]{1,0:T(8,128)S(1)} %get-tuple-element.164.selected_ref), channel_id=1, source_target_pairs={{0,1},{1,0},{2,3},{3,2},{4,5},{5,4},{6,7},{7,6},{8,9},{9,8},{10,11... | collective-permute-start | bytes 294920 | tf_op jit(solution)/shard_map/ppermute | solution.py:33
  29.8 4.3 %copy-start.10 = (f32[16,1024]{1,0:T(8,128)S(1)}, f32[16,1024]{1,0:T(8,128)}, u32[]{:S(2)}) copy-start(f32[16,1024]{1,0:T(8,128)} %decay_log_ref.7) | copy-start | bytes 196612
  29.9 4.3 %copy-start.19 = (bf16[64,1024]{1,0:T(8,128)(2,1)S(1)}, bf16[64,1024]{1,0:T(8,128)(2,1)}, u32[]{:S(2)}) copy-start(bf16[64,1024]{1,0:T(8,128)(2,1)} %step_weight_ref.1) | copy-start | bytes 393220
  34.1 30.0 %copy-start.31 = (f32[1024]{0:T(1024)S(1)}, f32[1024]{0:T(1024)}, u32[]{:S(2)}) copy-start(f32[1024]{0:T(1024)} %param.24) | copy-start | bytes 12292
  44.0 1.7 collective-permute-start.26
  48.3 6.6 %collective-permute-start.27 = (f32[40,1024]{1,0:T(8,128)}, f32[40,1024]{1,0:T(8,128)}, u32[]{:S(2)}, u32[]{:S(2)}) collective-permute-start(f32[40,1024]{1,0:T(8,128)} %get-tuple-element.169.own_ref), channel_id=1, source_target_pairs={{0,4},{2,6},{4,0},{6,2},{8,12},{10,14},{12,8},{14,10},{16,20},{18,... | collective-permute-start | bytes 491528 | tf_op jit(solution)/shard_map/ppermute | solution.py:33
  56.7 6.8 %collective-permute-start.28 = (f32[16,1024]{1,0:T(8,128)}, f32[16,1024]{1,0:T(8,128)S(1)}, u32[]{:S(2)}, u32[]{:S(2)}) collective-permute-start(f32[16,1024]{1,0:T(8,128)} %get-tuple-element.172), channel_id=1, source_target_pairs={{0,8},{2,10},{4,12},{6,14},{8,16},{10,18},{12,20},{14,22},{16,24},... | collective-permute-start | bytes 196616 | tf_op jit(solution)/shard_map/ppermute | solution.py:28
  64.1 9.8 %copy-start.9 = (bf16[272,1024]{1,0:T(8,128)(2,1)S(1)}, bf16[272,1024]{1,0:T(8,128)(2,1)}, u32[]{:S(2)}) copy-start(bf16[272,1024]{1,0:T(8,128)(2,1)} %get-tuple-element.162) | copy-start | bytes 1671172
  73.9 3.2 %copy-start.4 = (bf16[2,256,1024]{2,1,0:T(8,128)(2,1)S(1)}, bf16[2,256,1024]{2,1,0:T(8,128)(2,1)}, u32[]{:S(2)}) copy-start(bf16[2,256,1024]{2,1,0:T(8,128)(2,1)} %get-tuple-element.175) | copy-start | bytes 3145732
  79.9 5.4 %copy-start.39 = (f32[16,1024]{1,0:T(8,128)S(1)}, f32[16,1024]{1,0:T(8,128)}, u32[]{:S(2)}) copy-start(f32[16,1024]{1,0:T(8,128)} %get-tuple-element.174) | copy-start | bytes 196612
  80.4 6.2 %copy-start.5 = (bf16[2,256,1024]{2,1,0:T(8,128)(2,1)S(1)}, bf16[2,256,1024]{2,1,0:T(8,128)(2,1)}, u32[]{:S(2)}) copy-start(bf16[2,256,1024]{2,1,0:T(8,128)(2,1)} %get-tuple-element.175) | copy-start | bytes 3145732
  83.0 10.1 %copy-start.1 = (bf16[1024,1024]{1,0:T(8,128)(2,1)S(1)}, bf16[1024,1024]{1,0:T(8,128)(2,1)}, u32[]{:S(2)}) copy-start(bf16[1024,1024]{1,0:T(8,128)(2,1)} %param.25) | copy-start | bytes 6291460
  83.0 10.1 %copy-start.32 = (f32[1024]{0:T(1024)S(1)}, f32[1024]{0:T(1024)}, u32[]{:S(2)}) copy-start(f32[1024]{0:T(1024)} %param.16) | copy-start | bytes 12292
  85.3 7.8 %collective-permute-start.29 = (f32[16,1024]{1,0:T(8,128)S(1)}, f32[16,1024]{1,0:T(8,128)S(1)}, u32[]{:S(2)}, u32[]{:S(2)}) collective-permute-start(f32[16,1024]{1,0:T(8,128)S(1)} %copy-done.39), channel_id=1, source_target_pairs={{8,0},{10,2},{12,4},{14,6},{16,8},{18,10},{20,12},{22,14},{24,16},... | collective-permute-start | bytes 196616 | tf_op jit(solution)/shard_map/ppermute | solution.py:28
  93.0 0.8 copy-start.2
  95.5 33.5 %collective-permute-start.1 = (f32[256,512]{1,0:T(8,128)}, f32[256,512]{1,0:T(8,128)}, u32[]{:S(2)}, u32[]{:S(2)}) collective-permute-start(f32[256,512]{1,0:T(8,128)} %slice_select_fusion.1), channel_id=1, source_target_pairs={{0,1},{1,0},{2,3},{3,2},{4,5},{5,4},{6,7},{7,6},{8,9},{9,8},{10,11... | collective-permute-start | bytes 1572872 | tf_op jit(solution)/shard_map/cond/branch_1_fun/ppermute | solution.py:33
  98.1 26.8 %collective-permute-start.3 = (bf16[256,256]{1,0:T(8,128)(2,1)S(1)}, bf16[256,256]{1,0:T(8,128)(2,1)S(1)}, u32[]{:S(2)}, u32[]{:S(2)}) collective-permute-start(bf16[256,256]{1,0:T(8,128)(2,1)S(1)} %get-tuple-element.238), channel_id=1, source_target_pairs={{0,2},{2,0},{4,6},{6,4},{8,10},{10,8},{12,14},{14,12},{16,18},{18,... | collective-permute-start | bytes 393224 | tf_op jit(solution)/shard_map/cond/branch_1_fun/ppermute | solution.py:33
  98.2 26.7 %collective-permute-start.2 = (bf16[256,256]{1,0:T(8,128)(2,1)S(1)}, bf16[256,256]{1,0:T(8,128)(2,1)S(1)}, u32[]{:S(2)}, u32[]{:S(2)}) collective-permute-start(bf16[256,256]{1,0:T(8,128)(2,1)S(1)} %get-tuple-element.239), channel_id=1, source_target_pairs={{0,4},{2,6},{4,0},{6,2},{8,12},{10,14},{12,8},{14,10},{16,20},{18,... | collective-permute-start | bytes 393224 | tf_op jit(solution)/shard_map/cond/branch_1_fun/ppermute | solution.py:33
  98.8 26.1 %collective-permute-start.4 = (bf16[256,256]{1,0:T(8,128)(2,1)S(1)}, bf16[256,256]{1,0:T(8,128)(2,1)S(1)}, u32[]{:S(2)}, u32[]{:S(2)}) collective-permute-start(bf16[256,256]{1,0:T(8,128)(2,1)S(1)} %get-tuple-element.240), channel_id=1, source_target_pairs={{0,6},{2,4},{4,2},{6,0},{8,14},{10,12},{12,10},{14,8},{16,22},{18,... | collective-permute-start | bytes 393224 | tf_op jit(solution)/shard_map/cond/branch_1_fun/ppermute | solution.py:33
  100.0 29.6 %copy-start.3 = (bf16[256,1024]{1,0:T(8,128)(2,1)S(1)}, bf16[256,1024]{1,0:T(8,128)(2,1)}, u32[]{:S(2)}) copy-start(bf16[256,1024]{1,0:T(8,128)(2,1)} %copy-done.2) | copy-start | bytes 1572868 | tf_op jit(solution)/shard_map/cond
  100.0 29.6 %copy-start.13 = (f32[256,1024]{1,0:T(8,128)S(1)}, f32[256,1024]{1,0:T(8,128)}, u32[]{:S(2)}) copy-start(f32[256,1024]{1,0:T(8,128)} %get-tuple-element.87.convolved_ref) | copy-start | bytes 3145732 | tf_op jit(solution)/shard_map/cond
  100.0 29.6 %copy-start.16 = (bf16[96,1024]{1,0:T(8,128)(2,1)S(1)}, bf16[96,1024]{1,0:T(8,128)(2,1)}, u32[]{:S(2)}) copy-start(bf16[96,1024]{1,0:T(8,128)(2,1)} %get-tuple-element.85.select_ref) | copy-start | bytes 589828 | tf_op jit(solution)/shard_map/cond
  123.7 5.3 %collective-permute-start = (f32[96,256]{1,0:T(8,128)}, f32[96,256]{1,0:T(8,128)S(1)}, u32[]{:S(2)}, u32[]{:S(2)}) collective-permute-start(f32[96,256]{1,0:T(8,128)} %get-tuple-element.84.select_grad_ref), channel_id=1, source_target_pairs={{0,1},{1,0},{2,3},{3,2},{4,5},{5,4},{6,7},{7,6},{8,9},{9,8},{10,11... | collective-permute-start | bytes 294920 | tf_op jit(solution)/shard_map/cond/branch_1_fun/ppermute | solution.py:33
  129.6 6.8 %copy-start.24 = (f32[256,1]{1,0:T(8,128)S(1)}, f32[256,1]{1,0:T(8,128)}, u32[]{:S(2)}) copy-start(f32[256,1]{1,0:T(8,128)} %get-tuple-element.224) | copy-start | bytes 3076 | tf_op jit(solution)/shard_map/cond
  134.4 3.2 %collective-permute-start.5 = (f32[8,1024]{1,0:T(8,128)S(1)}, f32[8,1024]{1,0:T(8,128)S(1)}, u32[]{:S(2)}, u32[]{:S(2)}) collective-permute-start(f32[8,1024]{1,0:T(8,128)S(1)} %slice.40), channel_id=1, source_target_pairs={{2,0},{4,2},{6,4},{8,6},{10,8},{12,10},{14,12},{16,14},{18,16},{20... | collective-permute-start | bytes 98312 | tf_op jit(solution)/shard_map/cond/branch_1_fun/ppermute | solution.py:28
  138.5 7.1 %copy-start.8 = (bf16[256,1024]{1,0:T(8,128)(2,1)}, bf16[256,1024]{1,0:T(8,128)(2,1)S(1)}, u32[]{:S(2)}) copy-start(bf16[256,1024]{1,0:T(8,128)(2,1)S(1)} %get-tuple-element.236.own_ref) | copy-start | bytes 1572868 | tf_op jit(solution)/shard_map/cond
  138.6 17.5 %collective-permute-start.6 = (bf16[256,1024]{1,0:T(8,128)(2,1)S(1)}, bf16[256,1024]{1,0:T(8,128)(2,1)}, u32[]{:S(2)}, u32[]{:S(2)}) collective-permute-start(bf16[256,1024]{1,0:T(8,128)(2,1)S(1)} %get-tuple-element.236.own_ref), channel_id=1, source_target_pairs={{0,4},{2,6},{4,0},{6,2},{8,12},{10,14},{12,8},{14,10},{16,20},{18,... | collective-permute-start | bytes 1572872 | tf_op jit(solution)/shard_map/cond/branch_1_fun/ppermute | solution.py:33
  145.1 3.7 %copy-start.36 = (f32[1024]{0:T(1024)}, f32[1024]{0:T(1024)S(1)}, u32[]{:S(2)}) copy-start(f32[1024]{0:T(1024)S(1)} %get-tuple-element.230) | copy-start | bytes 12292 | tf_op jit(solution)/shard_map/cond
  145.1 3.7 %collective-permute-start.7 = (f32[1,1024]{1,0:T(1,128)S(1)}, f32[1,1024]{1,0:T(1,128)S(1)}, u32[]{:S(2)}, u32[]{:S(2)}) collective-permute-start(f32[1,1024]{1,0:T(1,128)S(1)} %bitcast.54), channel_id=1, source_target_pairs={{0,1},{1,0},{2,3},{3,2},{4,5},{5,4},{6,7},{7,6},{8,9},{9,8},{10,11... | collective-permute-start | bytes 12296 | tf_op jit(solution)/shard_map/cond/branch_1_fun/ppermute | solution.py:33
  145.6 27.2 %collective-permute-start.8 = (bf16[256,1024]{1,0:T(8,128)(2,1)S(1)}, bf16[256,1024]{1,0:T(8,128)(2,1)}, u32[]{:S(2)}, u32[]{:S(2)}) collective-permute-start(bf16[256,1024]{1,0:T(8,128)(2,1)S(1)} %get-tuple-element.236.own_ref), channel_id=1, source_target_pairs={{0,2},{2,0},{4,6},{6,4},{8,10},{10,8},{12,14},{14,12},{16,18},{18,... | collective-permute-start | bytes 1572872 | tf_op jit(solution)/shard_map/cond/branch_1_fun/ppermute | solution.py:33
  151.4 9.5 %copy-start.26 = (bf16[64,1024]{1,0:T(8,128)(2,1)S(1)}, bf16[64,1024]{1,0:T(8,128)(2,1)}, u32[]{:S(2)}) copy-start(bf16[64,1024]{1,0:T(8,128)(2,1)} %get-tuple-element.104.refs_2_) | copy-start | bytes 393220 | tf_op jit(solution)/shard_map/cond
  151.4 11.6 %copy-start.25 = (bf16[64,1024]{1,0:T(8,128)(2,1)S(1)}, bf16[64,1024]{1,0:T(8,128)(2,1)}, u32[]{:S(2)}) copy-start(bf16[64,1024]{1,0:T(8,128)(2,1)} %get-tuple-element.105.refs_3_) | copy-start | bytes 393220 | tf_op jit(solution)/shard_map/cond
  156.0 16.8 %collective-permute-start.9 = (bf16[256,1024]{1,0:T(8,128)(2,1)}, bf16[256,1024]{1,0:T(8,128)(2,1)}, u32[]{:S(2)}, u32[]{:S(2)}) collective-permute-start(bf16[256,1024]{1,0:T(8,128)(2,1)} %after.2.near_ref), channel_id=1, source_target_pairs={{0,2},{2,0},{4,6},{6,4},{8,10},{10,8},{12,14},{14,12},{16,18},{18,... | collective-permute-start | bytes 1572872 | tf_op jit(solution)/shard_map/cond/branch_1_fun/ppermute | solution.py:33
  157.3 3.6 %collective-permute-start.13 = (f32[1,256]{1,0:T(1,128)S(1)}, f32[1,256]{1,0:T(1,128)S(1)}, u32[]{:S(2)}, u32[]{:S(2)}) collective-permute-start(f32[1,256]{1,0:T(1,128)S(1)} %bitcast.59), channel_id=1, source_target_pairs={{0,1},{1,0},{2,3},{3,2},{4,5},{5,4},{6,7},{7,6},{8,9},{9,8},{10,11... | collective-permute-start | bytes 3080 | tf_op jit(solution)/shard_map/cond/branch_1_fun/ppermute | solution.py:33
  157.9 5.1 %collective-permute-start.10 = (bf16[64,1024]{1,0:T(8,128)(2,1)}, bf16[64,1024]{1,0:T(8,128)(2,1)S(1)}, u32[]{:S(2)}, u32[]{:S(2)}) collective-permute-start(bf16[64,1024]{1,0:T(8,128)(2,1)} %get-tuple-element.103.refs_1_), channel_id=1, source_target_pairs={{0,2},{2,0},{4,6},{6,4},{8,10},{10,8},{12,14},{14,12},{16,18},{18,... | collective-permute-start | bytes 393224 | tf_op jit(solution)/shard_map/cond/branch_1_fun/ppermute | solution.py:33
  158.8 47.0 %collective-permute-start.20 = (f32[256,512]{1,0:T(8,128)}, f32[256,512]{1,0:T(8,128)}, u32[]{:S(2)}, u32[]{:S(2)}) collective-permute-start(f32[256,512]{1,0:T(8,128)} %slice_select_fusion), channel_id=1, source_target_pairs={{0,1},{1,0},{2,3},{3,2},{4,5},{5,4},{6,7},{7,6},{8,9},{9,8},{10,11... | collective-permute-start | bytes 1572872 | tf_op jit(solution)/shard_map/cond/branch_1_fun/ppermute | solution.py:33
  160.9 11.9 %copy-start.35 = (f32[1,256]{1,0:T(1,128)}, f32[1,256]{1,0:T(1,128)S(1)}, u32[]{:S(2)}) copy-start(f32[1,256]{1,0:T(1,128)S(1)} %collective-permute-done.13.rest_0_) | copy-start | bytes 3076 | tf_op jit(solution)/shard_map/cond
  160.9 7.7 %collective-permute-start.11 = (bf16[64,1024]{1,0:T(8,128)(2,1)S(1)}, bf16[64,1024]{1,0:T(8,128)(2,1)S(1)}, u32[]{:S(2)}, u32[]{:S(2)}) collective-permute-start(bf16[64,1024]{1,0:T(8,128)(2,1)S(1)} %copy-done.26), channel_id=1, source_target_pairs={{0,4},{2,6},{4,0},{6,2},{8,12},{10,14},{12,8},{14,10},{16,20},{18,... | collective-permute-start | bytes 393224 | tf_op jit(solution)/shard_map/cond/branch_1_fun/ppermute | solution.py:33
  163.0 9.8 %copy-start.21 = (bf16[64,1024]{1,0:T(8,128)(2,1)}, bf16[64,1024]{1,0:T(8,128)(2,1)S(1)}, u32[]{:S(2)}) copy-start(bf16[64,1024]{1,0:T(8,128)(2,1)S(1)} %collective-permute-done.10.first_ref) | copy-start | bytes 393220 | tf_op jit(solution)/shard_map/cond
  163.0 9.8 %collective-permute-start.12 = (bf16[64,1024]{1,0:T(8,128)(2,1)S(1)}, bf16[64,1024]{1,0:T(8,128)(2,1)S(1)}, u32[]{:S(2)}, u32[]{:S(2)}) collective-permute-start(bf16[64,1024]{1,0:T(8,128)(2,1)S(1)} %copy-done.25), channel_id=1, source_target_pairs={{0,6},{2,4},{4,2},{6,0},{8,14},{10,12},{12,10},{14,8},{16,22},{18,... | collective-permute-start | bytes 393224 | tf_op jit(solution)/shard_map/cond/branch_1_fun/ppermute | solution.py:33
  168.6 4.2 %copy-start.22 = (bf16[64,1024]{1,0:T(8,128)(2,1)}, bf16[64,1024]{1,0:T(8,128)(2,1)S(1)}, u32[]{:S(2)}) copy-start(bf16[64,1024]{1,0:T(8,128)(2,1)S(1)} %collective-permute-done.11.second_ref) | copy-start | bytes 393220 | tf_op jit(solution)/shard_map/cond
  173.5 32.3 %copy-start.7 = (bf16[256,512]{1,0:T(8,128)(2,1)S(1)}, bf16[256,512]{1,0:T(8,128)(2,1)}, u32[]{:S(2)}) copy-start(bf16[256,512]{1,0:T(8,128)(2,1)} %get-tuple-element.112) | copy-start | bytes 786436 | tf_op jit(solution)/shard_map/cond
  173.5 32.3 %copy-start.12 = (bf16[256,512]{1,0:T(8,128)(2,1)S(1)}, bf16[256,512]{1,0:T(8,128)(2,1)}, u32[]{:S(2)}) copy-start(bf16[256,512]{1,0:T(8,128)(2,1)} %get-tuple-element.113) | copy-start | bytes 786436 | tf_op jit(solution)/shard_map/cond
  177.1 14.0 %collective-permute-start.14 = (bf16[80,1024]{1,0:T(8,128)(2,1)}, bf16[80,1024]{1,0:T(8,128)(2,1)S(1)}, u32[]{:S(2)}, u32[]{:S(2)}) collective-permute-start(bf16[80,1024]{1,0:T(8,128)(2,1)} %get-tuple-element.109), channel_id=1, source_target_pairs={{0,8},{2,10},{4,12},{6,14},{8,0},{10,2},{12,4},{14,6},{16,24},{18,... | collective-permute-start | bytes 491528 | tf_op jit(solution)/shard_map/cond/branch_1_fun/ppermute | solution.py:33
  178.4 13.6 %collective-permute-start.15 = (bf16[80,1024]{1,0:T(8,128)(2,1)}, bf16[80,1024]{1,0:T(8,128)(2,1)S(1)}, u32[]{:S(2)}, u32[]{:S(2)}) collective-permute-start(bf16[80,1024]{1,0:T(8,128)(2,1)} %get-tuple-element.110), channel_id=1, source_target_pairs={{0,16},{2,18},{4,20},{6,22},{8,24},{10,26},{12,28},{14,30},{16,0},... | collective-permute-start | bytes 491528 | tf_op jit(solution)/shard_map/cond/branch_1_fun/ppermute | solution.py:33
  180.1 22.9 %collective-permute-start.16 = (bf16[80,1024]{1,0:T(8,128)(2,1)}, bf16[80,1024]{1,0:T(8,128)(2,1)S(1)}, u32[]{:S(2)}, u32[]{:S(2)}) collective-permute-start(bf16[80,1024]{1,0:T(8,128)(2,1)} %get-tuple-element.111), channel_id=1, source_target_pairs={{0,24},{2,26},{4,28},{6,30},{8,16},{10,18},{12,20},{14,22},{16,8},... | collective-permute-start | bytes 491528 | tf_op jit(solution)/shard_map/cond/branch_1_fun/ppermute | solution.py:33
  204.1 11.2 %collective-permute-start.19 = (bf16[80,1024]{1,0:T(8,128)(2,1)S(1)}, bf16[80,1024]{1,0:T(8,128)(2,1)S(1)}, u32[]{:S(2)}, u32[]{:S(2)}) collective-permute-start(bf16[80,1024]{1,0:T(8,128)(2,1)S(1)} %add_convert_fusion), channel_id=1, source_target_pairs={{0,8},{2,10},{4,12},{6,14},{8,0},{10,2},{12,4},{14,6},{16,24},{18,... | collective-permute-start | bytes 491528 | tf_op jit(solution)/shard_map/cond/branch_1_fun/ppermute | solution.py:33
  208.0 14.3 %collective-permute-start.18 = (bf16[80,1024]{1,0:T(8,128)(2,1)S(1)}, bf16[80,1024]{1,0:T(8,128)(2,1)S(1)}, u32[]{:S(2)}, u32[]{:S(2)}) collective-permute-start(bf16[80,1024]{1,0:T(8,128)(2,1)S(1)} %add_convert_fusion), channel_id=1, source_target_pairs={{0,16},{2,18},{4,20},{6,22},{8,24},{10,26},{12,28},{14,30},{16,0},... | collective-permute-start | bytes 491528 | tf_op jit(solution)/shard_map/cond/branch_1_fun/ppermute | solution.py:33
  209.2 13.1 %collective-permute-start.17 = (bf16[80,1024]{1,0:T(8,128)(2,1)S(1)}, bf16[80,1024]{1,0:T(8,128)(2,1)S(1)}, u32[]{:S(2)}, u32[]{:S(2)}) collective-permute-start(bf16[80,1024]{1,0:T(8,128)(2,1)S(1)} %add_convert_fusion), channel_id=1, source_target_pairs={{0,24},{2,26},{4,28},{6,30},{8,16},{10,18},{12,20},{14,22},{16,8},... | collective-permute-start | bytes 491528 | tf_op jit(solution)/shard_map/cond/branch_1_fun/ppermute | solution.py:33
  223.3 7.2 %collective-permute-start.31 = (bf16[320,1024]{1,0:T(8,128)(2,1)}, bf16[320,1024]{1,0:T(8,128)(2,1)S(1)}, u32[]{:S(2)}, u32[]{:S(2)}) collective-permute-start(bf16[320,1024]{1,0:T(8,128)(2,1)} %get-tuple-element.181.inner_ref), channel_id=1, source_target_pairs={{0,2},{2,0},{4,6},{6,4},{8,10},{10,8},{12,14},{14,12},{16,18},{18,... | collective-permute-start | bytes 1966088 | tf_op jit(solution)/shard_map/ppermute | solution.py:33
  223.3 17.4 %collective-permute-start.30 = (bf16[320,1024]{1,0:T(8,128)(2,1)}, bf16[320,1024]{1,0:T(8,128)(2,1)S(1)}, u32[]{:S(2)}, u32[]{:S(2)}) collective-permute-start(bf16[320,1024]{1,0:T(8,128)(2,1)} %get-tuple-element.181.inner_ref), channel_id=1, source_target_pairs={{0,4},{2,6},{4,0},{6,2},{8,12},{10,14},{12,8},{14,10},{16,20},{18,... | collective-permute-start | bytes 1966088 | tf_op jit(solution)/shard_map/ppermute | solution.py:33
  230.6 0.8 copy-start.17
  240.7 0.8 copy-start.6
  241.5 2.7 %collective-permute-start.32 = (bf16[320,1024]{1,0:T(8,128)(2,1)}, bf16[320,1024]{1,0:T(8,128)(2,1)S(1)}, u32[]{:S(2)}, u32[]{:S(2)}) collective-permute-start(bf16[320,1024]{1,0:T(8,128)(2,1)} %after.3.inner_ref), channel_id=1, source_target_pairs={{0,2},{2,0},{4,6},{6,4},{8,10},{10,8},{12,14},{14,12},{16,18},{18,... | collective-permute-start | bytes 1966088 | tf_op jit(solution)/shard_map/ppermute | solution.py:33
  244.2 0.8 copy-start.18
  (10 other events, 6.6 us)
Sparse Core Ops, SparseCore 0:
  79.3 137.1 all-reduce.2

commit v10 on v9

--- a/solution.py
+++ b/solution.py
@@ -99,9 +99,7 @@
     def quarter(n):
         return lax.dynamic_slice_in_dim(array, (here ^ n) * width, width, 1)
 
-    return jnp.stack(
-        [quarter(0)] + [swapped(quarter(n), "wide", n) for n in (2, 1, 3)]
-    )
+    return [quarter(0)] + [swapped(quarter(n), "wide", n) for n in (2, 1, 3)]
 
 
 def silu_slope(values):
@@ -358,7 +356,9 @@
     passed_ref,
     entering_ref,
     skip_ref,
-    pair_ref,
+    wait_ref,
+    gated_ref,
+    gate_grad_ref,
     entry_ref,
     coef,
     held_step,
@@ -393,13 +393,13 @@
     gate = gate_ref[...].astype(f32)
     logistic = jax.nn.sigmoid(gate)
     total = scanned[...] + skip_ref[...] * act
-    pair_ref[0] = (total * (gate * logistic)).astype(bf16)
+    gated_ref[...] = (total * (gate * logistic)).astype(bf16)
     slope = logistic * (1.0 + gate * (1.0 - logistic))
-    pair_ref[1] = (gated_grad_ref[...] * total * slope).astype(bf16)
+    gate_grad_ref[...] = (gated_grad_ref[...] * total * slope).astype(bf16)
 
 
 def scan_forward(
-    selected, other, step, act, projected, gated_grad, masks, decay_log, passed, entering, skip_gain
+    selected, other, step, act, projected, gated_grad, masks, decay_log, passed, entering, skip_gain, wait
 ):
     rows, width = step.shape
     count = decay_log.shape[0]
@@ -420,10 +420,12 @@
             column_spec(2 * count + 8),
             column_spec(count),
             column_spec(1),
+            pl.BlockSpec(memory_space=pl.ANY),
         ],
-        [pl.BlockSpec((2, rows, scan_width), lambda j: (0, 0, j)), column_spec(count)],
+        [column_spec(rows), column_spec(rows), column_spec(count)],
         [
-            jax.ShapeDtypeStruct((2, rows, width), bf16),
+            jax.ShapeDtypeStruct((rows, width), bf16),
+            jax.ShapeDtypeStruct((rows, width), bf16),
             jax.ShapeDtypeStruct((count, width), f32),
         ],
         [pltpu.VMEM((2 * count, rows), f32)]
@@ -440,6 +442,7 @@
         passed,
         entering,
         skip_gain,
+        wait,
     )
 
 
@@ -545,8 +548,6 @@
     small_ref[rank : rank + count, :] = decay_grad * decay
     bias_grad = jnp.sum(pre_grad.astype(f32), axis=0, keepdims=True)
     small_ref[rank + count + 1 : rank + count + 2, :] = bias_grad
-    spare = small_ref.shape[0] - (rank + count + 2)
-    small_ref[rank + count + 2 :, :] = jnp.zeros((spare, small_ref.shape[1]), f32)
     select_grad_ref[:rank, :] += lax.dot_general(
         step_weight_ref[...], pre_grad, contract_last, preferred_element_type=f32
     )
@@ -580,7 +581,7 @@
     columns = selected.shape[0]
     rank = step_weight.shape[0]
     half_rows = 8 * body_rows * (scan_width // lanes)
-    small = rank + count + 16
+    small = rank + count + 2
     return call(
         backward_kernel,
         "scan_backward",
@@ -646,7 +647,7 @@
     mask_ref,
     *rest,
 ):
-    inner_grad_ref, edge_ref, small_ref, inner, shifted = rest[-5:]
+    inner_grad_ref, before_ref, last_ref, small_ref, inner, shifted = rest[-6:]
     rows = act_ref.shape[0]
     taps = conv_weight_ref.shape[0]
     columns = select_ref.shape[0]
@@ -677,11 +678,9 @@
         out = out + weight * shifted[pl.ds(8 + lag, rows), :]
         before = before + weight * shifted[pl.ds(lag, 8), :]
     small_ref[columns + taps : columns + taps + 1, :] = jnp.sum(conv_grad, axis=0, keepdims=True)
-    spare = small_ref.shape[0] - (columns + taps + 1)
-    small_ref[columns + taps + 1 :, :] = jnp.zeros((spare, small_ref.shape[1]), f32)
     inner_grad_ref[...] = out.astype(bf16)
-    edge_ref[:8, :] = before
-    edge_ref[8:, :] = out[rows - 8 :, :]
+    before_ref[...] = before
+    last_ref[...] = out[rows - 8 :, :]
 
 
 def convolve_grad(
@@ -691,7 +690,7 @@
     extended = rows + halo
     columns = select_weight.shape[0]
     taps = conv_weight.shape[0]
-    small = columns + 16
+    small = columns + taps + 1
     return call(
         conv_grad_kernel,
         "convolve_grad",
@@ -708,10 +707,11 @@
             whole_spec(rows, masks.shape[1]),
         ]
         + [pl.BlockSpec(memory_space=pl.ANY)] * len(waits),
-        [column_spec(rows), column_spec(16), column_spec(small)],
+        [column_spec(rows), column_spec(8), column_spec(8), column_spec(small)],
         [
             jax.ShapeDtypeStruct((rows, width), bf16),
-            jax.ShapeDtypeStruct((16, width), f32),
+            jax.ShapeDtypeStruct((8, width), f32),
+            jax.ShapeDtypeStruct((8, width), f32),
             jax.ShapeDtypeStruct((small, width), f32),
         ],
         [pltpu.VMEM((extended, scan_width), f32), pltpu.VMEM((rows + 16, scan_width), f32)],
@@ -736,9 +736,11 @@
     gain_ref,
     ids_ref,
     whole_ref,
+    extended_ref,
     normed_ref,
     inverse_ref,
     mask_ref,
+    rows_ref,
 ):
     rows, half = own_ref.shape
     ids = ids_ref[...].astype(f32)
@@ -752,11 +754,14 @@
     right = lax.axis_index("narrow") == 1
     for at, own, other in ((0, own_ref, other_ref), (rows, edge_ref, other_edge_ref)):
         end = at + own.shape[0]
-        whole_ref[at:end, :half] = jnp.where(right, other[...], own[...])
-        whole_ref[at:end, half:] = jnp.where(right, own[...], other[...])
-    whole = whole_ref[...].astype(f32)
+        rows_ref[at:end, :half] = jnp.where(right, other[...], own[...])
+        rows_ref[at:end, half:] = jnp.where(right, own[...], other[...])
+    whole_ref[...] = rows_ref[:rows, :]
+    whole = rows_ref[...].astype(f32)
     inverse = lax.rsqrt(jnp.mean(whole * whole, axis=1, keepdims=True) + epsilon)
-    normed_ref[...] = (whole * inverse * gain_ref[...]).astype(bf16)
+    normed = (whole * inverse * gain_ref[...]).astype(bf16)
+    extended_ref[...] = normed
+    normed_ref[...] = normed[:rows]
     inverse_ref[...] = inverse[:rows]
 
 
@@ -766,11 +771,13 @@
     return pl.pallas_call(
         normalize_kernel,
         out_shape=[
+            jax.ShapeDtypeStruct((rows, 2 * half), bf16),
             jax.ShapeDtypeStruct((extended, 2 * half), bf16),
-            jax.ShapeDtypeStruct((extended, 2 * half), bf16),
+            jax.ShapeDtypeStruct((rows, 2 * half), bf16),
             jax.ShapeDtypeStruct((rows, 1), f32),
             jax.ShapeDtypeStruct((rows, lanes), f32),
         ],
+        scratch_shapes=[pltpu.VMEM((extended, 2 * half), bf16)],
         cost_estimate=tiny_cost,
         name="normalized",
     )(own, other, edge, other_edge, gain, ids)
@@ -787,6 +794,34 @@
         cost_estimate=tiny_cost,
         name="after",
     )(array, *waits)
+
+
+def patch_kernel(ids_ref, rows_ref, last_ref, next_ref, out_ref):
+    count = ids_ref.shape[0]
+    place = lax.broadcasted_iota(jnp.int32, (8, 1), 0)
+    same = jnp.zeros((8, 1), f32)
+    for lag in range(8):
+        here = jnp.where(ids_ref[count - 1 - lag] == ids_ref[count - 1], 1.0, 0.0)
+        same = same + jnp.where(place == 7 - lag, here, 0.0)
+    total = last_ref[...] + next_ref[...] * same
+    rows = rows_ref[...].astype(f32)
+    out_ref[...] = jnp.concatenate([rows[: halo - 8], total]).astype(bf16)
+
+
+def patched(ids, grads, last, following):
+    rows, width = grads.shape
+    block = pl.BlockSpec((halo, width), lambda j: (rows // halo - 1, 0))
+    edge = pl.BlockSpec((8, width), lambda j: (0, 0))
+    return pl.pallas_call(
+        patch_kernel,
+        grid=(1,),
+        in_specs=[pl.BlockSpec(memory_space=pltpu.SMEM), block, edge, edge],
+        out_specs=block,
+        out_shape=jax.ShapeDtypeStruct((rows, width), bf16),
+        input_output_aliases={1: 0},
+        cost_estimate=tiny_cost,
+        name="patched",
+    )(ids, grads, last, following)
 
 
 def edge_kernel(ids_ref, tokens_ref, out_ref):
@@ -817,38 +852,44 @@
     )(ids, tokens)
 
 
-def small_kernel(place_ref, scan_ref, conv_ref, gain_ref, other_gain_ref, keep_ref, *rest):
-    sends_refs, rows = rest[:3], rest[3]
-    at = 0
-    for ref in (scan_ref, conv_ref):
-        rows[at : at + ref.shape[0], :] = ref[...]
-        at += ref.shape[0]
-    rows[at:, :] = jnp.broadcast_to(
-        gain_ref[...] + other_gain_ref[...], (rows.shape[0] - at, rows.shape[1])
-    )
+block_rows, used_rows = 16, 12
+
+
+def small_kernel(place_ref, scan_ref, conv_ref, keep_ref, *rest):
+    *sends_refs, rows, blocks = rest
+    rows[...] = jnp.zeros(rows.shape, f32)
+    rows[: scan_ref.shape[0], :] = scan_ref[...]
+    rows[scan_ref.shape[0] : scan_ref.shape[0] + conv_ref.shape[0], :] = conv_ref[...]
+    blocks[...] = jnp.zeros(blocks.shape, f32)
+    for n in range(16):
+        blocks[n * block_rows : n * block_rows + used_rows, :] = rows[
+            n * used_rows : (n + 1) * used_rows, :
+        ]
     quarter = keep_ref.shape[0]
     for n in range(4):
         start = pl.multiple_of((place_ref[0] ^ n) * quarter, quarter)
-        block = rows[pl.ds(start, quarter), :]
+        block = blocks[pl.ds(start, quarter), :]
         if n == 0:
             keep_ref[...] = block
         else:
             sends_refs[n - 1][...] = block.astype(bf16)
 
 
-def small_quarters(place, scan_small, conv_small, gain, other_gain):
+def small_quarters(place, scan_small, conv_small):
     width = scan_small.shape[1]
-    rows = -(-(scan_small.shape[0] + conv_small.shape[0] + 1) // 256) * 256
     return pl.pallas_call(
         small_kernel,
         in_specs=[pl.BlockSpec(memory_space=pltpu.SMEM)]
-        + [pl.BlockSpec(memory_space=pltpu.VMEM)] * 4,
-        out_shape=[jax.ShapeDtypeStruct((rows // 4, width), f32)]
-        + [jax.ShapeDtypeStruct((rows // 4, width), bf16)] * 3,
-        scratch_shapes=[pltpu.VMEM((rows, width), f32)],
+        + [pl.BlockSpec(memory_space=pltpu.VMEM)] * 2,
+        out_shape=[jax.ShapeDtypeStruct((4 * block_rows, width), f32)]
+        + [jax.ShapeDtypeStruct((4 * block_rows, width), bf16)] * 3,
+        scratch_shapes=[
+            pltpu.VMEM((16 * used_rows, width), f32),
+            pltpu.VMEM((16 * block_rows, width), f32),
+        ],
         cost_estimate=tiny_cost,
         name="small_quarters",
-    )(place, scan_small, conv_small, gain, other_gain)
+    )(place, scan_small, conv_small)
 
 
 def quarter_kernel(
@@ -857,7 +898,10 @@
     near_ref,
     far_ref,
     last_ref,
-    normed_ref,
+    normed_0,
+    normed_1,
+    normed_2,
+    normed_3,
     small_ref,
     first_ref,
     second_ref,
@@ -866,8 +910,9 @@
 ):
     keep_ref, *sends_refs, piece, small = rest[-6:]
     total = None
-    for n, grads in enumerate((own_ref, near_ref, far_ref, last_ref)):
-        part = lax.dot_general(normed_ref[n], grads[...], contract_first, preferred_element_type=f32)
+    grads = (own_ref, near_ref, far_ref, last_ref)
+    for left, right in zip((normed_0, normed_1, normed_2, normed_3), grads):
+        part = lax.dot_general(left[...], right[...], contract_first, preferred_element_type=f32)
         total = part if total is None else total + part
     piece[...] = total
     small[...] = small_ref[...] + sum(
@@ -888,13 +933,13 @@
 
 def inner_quarter(place, own, near, far, last, normed, smalls, waits):
     width = own.shape[1]
-    quarter = normed.shape[2]
+    quarter = normed[0].shape[1]
     spare = smalls[0].shape[0]
     rows = (quarter + spare) // 4
     return pl.pallas_call(
         quarter_kernel,
         in_specs=[pl.BlockSpec(memory_space=pltpu.SMEM)]
-        + [pl.BlockSpec(memory_space=pltpu.VMEM)] * 9
+        + [pl.BlockSpec(memory_space=pltpu.VMEM)] * 12
         + [pl.BlockSpec(memory_space=pl.ANY)] * len(waits),
         out_shape=[jax.ShapeDtypeStruct((rows, width), f32)]
         + [jax.ShapeDtypeStruct((rows, width), bf16)] * 3,
@@ -902,66 +947,83 @@
         compiler_params=pltpu.CompilerParams(vmem_limit_bytes=vmem_bytes),
         cost_estimate=tiny_cost,
         name="inner_quarter",
-    )(place, own, near, far, last, normed, *smalls, *waits)
-
-
-def join_kernel(place_ref, gate_ref, inner_ref, *rest):
-    out_ref, small_ref = rest[-2:]
-    rows, spare = out_ref.shape[0] // 2, small_ref.shape[0] // 2
+    )(place, own, near, far, last, *normed, *smalls, *waits)
+
+
+def join_kernel(place_ref, gate_ref, first_ref, second_ref, *rest, small_rows):
+    at_end = 2 + len(small_rows) if small_rows else 0
+    out_ref = rest[-1 - at_end]
+    step = pl.program_id(0)
+    rows = out_ref.shape[0] // 2
     out_ref[:, 1, :] = gate_ref[...].astype(f32)
-    for n in range(2):
-        at = n * (rows + spare)
-        block = inner_ref[at : at + rows + spare, :].astype(f32)
-        out_ref[n * rows : (n + 1) * rows, 0, :] = block[:rows]
-        small_ref[n * spare : (n + 1) * spare, :] = block[rows:]
-
-
-def joined(place, flip, gate, inner, before, waits):
+
+    def put(ref):
+        for n in range(2):
+            at = n * (rows + block_rows)
+            out_ref[n * rows : (n + 1) * rows, 0, :] = ref[at : at + rows, :].astype(f32)
+
+    @pl.when(step < 2)
+    def _():
+        put(first_ref)
+
+    @pl.when(step >= 2)
+    def _():
+        put(second_ref)
+
+    if not small_rows:
+        return
+    *row_refs, gain_ref, blocks = rest[-at_end:]
+
+    @pl.when(step == 3)
+    def _():
+        for flip, ref in enumerate(rest[:4]):
+            for n in range(4):
+                at = ((place_ref[0] ^ flip) * 4 + n) * block_rows
+                taken = ref[(n + 1) * rows + n * block_rows : (n + 1) * (rows + block_rows), :]
+                blocks[pl.ds(pl.multiple_of(at, block_rows), block_rows), :] = taken.astype(f32)
+        for ref, start in zip(row_refs, small_rows):
+            for row in range(ref.shape[0]):
+                at = (start + row) // used_rows * block_rows + (start + row) % used_rows
+                ref[row : row + 1, :] = blocks[at : at + 1, :]
+        gain_ref[...] = sum(
+            blocks[n * block_rows + used_rows : n * block_rows + used_rows + 1, :] for n in range(16)
+        )
+
+
+def joined(place, flip, gate, first, second, before, waits, held=(), small_rows=(), small_counts=()):
     depth, width = gate.shape
     quarter = depth // 4
-    small = inner.shape[0] - quarter
+    block = quarter // 2
+    piece = first.shape[0] // 2
+
+    def target(j, place):
+        return 2 * (place[0] ^ (flip + j // 2)) + lax.rem(j, 2)
+
+    vmem = pl.BlockSpec(memory_space=pltpu.VMEM)
     untouched = [*before, *waits]
     return pl.pallas_call(
-        join_kernel,
+        functools.partial(join_kernel, small_rows=small_rows),
         grid_spec=pltpu.PrefetchScalarGridSpec(
             num_scalar_prefetch=1,
-            grid=(2,),
+            grid=(4,),
             in_specs=[
-                pl.BlockSpec((quarter // 2, width), lambda j, place: (2 * (place[0] ^ flip) + j, 0)),
-                pl.BlockSpec((inner.shape[0] // 2, width), lambda j, place: (j, 0)),
+                pl.BlockSpec((block, width), lambda j, place: (target(j, place), 0)),
+                pl.BlockSpec((piece, width), lambda j, place: (jnp.minimum(j, 1), 0)),
+                pl.BlockSpec((piece, width), lambda j, place: (jnp.maximum(j - 2, 0), 0)),
             ]
+            + [vmem] * len(held)
             + [pl.BlockSpec(memory_space=pl.ANY)] * len(untouched),
-            out_specs=[
-                pl.BlockSpec(
-                    (quarter // 2, 2, width), lambda j, place: (2 * (place[0] ^ flip) + j, 0, 0)
-                ),
-                pl.BlockSpec((small // 2, width), lambda j, place: (2 * (place[0] ^ flip) + j, 0)),
-            ],
+            out_specs=[pl.BlockSpec((block, 2, width), lambda j, place: (target(j, place), 0, 0))]
+            + [pl.BlockSpec((rows, width), lambda j, place: (0, 0)) for rows in small_counts],
+            scratch_shapes=[pltpu.VMEM((16 * block_rows, width), f32)] if small_rows else [],
         ),
-        out_shape=[
-            jax.ShapeDtypeStruct((depth, 2, width), f32),
-            jax.ShapeDtypeStruct((4 * small, width), f32),
-        ],
-        input_output_aliases={3 + k: k for k in range(len(before))},
+        out_shape=[jax.ShapeDtypeStruct((depth, 2, width), f32)]
+        + [jax.ShapeDtypeStruct((rows, width), f32) for rows in small_counts],
+        input_output_aliases={4 + len(held) + k: k for k in range(len(before))},
         compiler_params=pltpu.CompilerParams(vmem_limit_bytes=vmem_bytes),
         cost_estimate=tiny_cost,
         name="joined",
-    )(place, gate, inner, *untouched)
-
-
-def parts_kernel(small_ref, *out_refs, starts):
-    for ref, start in zip(out_refs, starts):
-        ref[...] = small_ref[start : start + ref.shape[0], :]
-
-
-def small_parts(small, sizes):
-    width = small.shape[1]
-    return pl.pallas_call(
-        functools.partial(parts_kernel, starts=[start for start, _ in sizes]),
-        out_shape=[jax.ShapeDtypeStruct((rows, width), f32) for _, rows in sizes],
-        cost_estimate=tiny_cost,
-        name="small_parts",
-    )(small)
+    )(place, gate, first, second, *held, *untouched)
 
 
 def through(decay, total):
@@ -1050,8 +1112,7 @@
     other_cot = swapped(cotangent, "narrow", 1)
     edge, other_edge = to_next_both(edge_rows_of(segment_ids, tokens))
 
-    same_as_last = (segment_ids[rows - 8 :] == segment_ids[rows - 1 :])[:, None]
-    whole_ext, normed_ext, inverse, masks = normalized(
+    whole_low, normed_ext, normed, inverse, masks = normalized(
         tokens, other_tokens, edge, other_edge, norm_gain[None], segment_ids[None]
     )
     projected = jnp.einsum(
@@ -1077,7 +1138,7 @@
         decay_log,
     )
     passed, entering, returning = carried(ends, decay_log)
-    pair, entry = scan_forward(
+    gated, gate_grad, entry = scan_forward(
         selected,
         other_selected,
         step,
@@ -1089,15 +1150,13 @@
         passed,
         entering,
         skip_gain[None],
-    )
-    gated, gate_grad = pair[0], pair[1]
-    normed = normed_ext[:rows]
+        returning,
+    )
     products = (
         lax.dot_general(gated, cot_whole, contract_first, preferred_element_type=f32).astype(bf16),
         lax.dot_general(normed, gate_grad, contract_first, preferred_element_type=f32).astype(bf16),
     )
     out_sum, gate_sum = lax.psum(products, "wide")
-    whole = whole_ext[:rows].astype(f32)
     wide_place = lax.axis_index("wide").astype(jnp.int32)
     four_place = (wide_place & 3)[None]
 
@@ -1106,6 +1165,7 @@
         return jnp.where(right_half, high, low), jnp.where(right_half, low, high)
 
     def after_forward(products):
+        whole = whole_low.astype(f32)
         normed_four = quarter_of_four(normed)
         out_part = jnp.dot(gated, out_weight, preferred_element_type=f32)
         out_mine, out_other = narrow_halves(out_part)
@@ -1127,7 +1187,7 @@
             step_weight,
         )
         layer_out = (tokens.astype(f32) + (out_mine + out_theirs)).astype(bf16)
-        inner_main, edges, conv_small = convolve_grad(
+        inner_main, before, last, conv_small = convolve_grad(
             select_grad,
             swapped(select_grad, "narrow", 1),
             select_weight,
@@ -1137,26 +1197,22 @@
             projected,
             conv_weight,
             masks,
-            [out_theirs, normed_four],
+            [out_theirs, *normed_four],
         )
-        from_next = passed_along(edges[:8], "wide", -1)
-        last_rows = edges[8:] + jnp.where(same_as_last, from_next, 0.0)
-        inner_grad = jnp.concatenate([inner_main[: rows - 8], last_rows.astype(bf16)])
+        inner_grad = patched(segment_ids, inner_main, last, passed_along(before, "wide", -1))
         near = swapped(inner_grad, "wide", 2)
         far = swapped(inner_grad, "wide", 1)
+        keep, *sends = small_quarters(four_place, scan_small, conv_small)
+        smalls = [keep] + [swapped(sends[n - 1], "wide", n) for n in (1, 2, 3)]
         normed_part = jnp.einsum(
             "cte,dce->td", jnp.stack([inner_grad, gate_grad]), in_weight, preferred_element_type=f32
         )
         gain_part = jnp.sum(normed_part * whole * inverse, axis=0, keepdims=True)
         row_part = jnp.sum(normed_part * norm_gain * whole, axis=1)[None]
-        keep, *sends = small_quarters(
-            four_place, scan_small, conv_small, gain_part, swapped(gain_part, "narrow", 1)
-        )
-        smalls = [keep] + [swapped(sends[n - 1], "wide", n) for n in (1, 2, 3)]
         normed_mine, normed_other = narrow_halves(normed_part)
         row_theirs = swapped(row_part, "narrow", 1)
         normed_theirs = swapped(normed_other, "narrow", 1)
-        near = after(near, *sends)
+        near = after(near, *smalls[1:])
         keep, *sends = inner_quarter(
             (wide_place >> 2 & 3)[None],
             inner_grad,
@@ -1174,14 +1230,20 @@
         ) * (row_sum / (2 * features))
         tokens_grad = (whole_grad + cotangent.astype(f32)).astype(bf16)
         first_bits, *more_bits = group_bits(2)
+        gain_sum = gain_part + swapped(gain_part, "narrow", 1)
+        for bit in (bit for bits in more_bits for bit in bits):
+            gain_sum = gain_sum + swapped(gain_sum, "wide", bit)
         held = keep
         for n, flip in enumerate(flips(first_bits)[1:]):
             held = held + swapped(sends[n], "wide", flip).astype(f32)
         for bits in more_bits:
             held = scattered(held, bits)
         held = held.astype(bf16)
-        for bits in reversed(group_bits(2)):
+        for bits in reversed(more_bits):
             held = gathered(held, bits)
+        spare = jnp.broadcast_to(gain_sum, (block_rows - used_rows, gain_sum.shape[1]))
+        held = jnp.concatenate([held[: held.shape[0] - spare.shape[0]], spare.astype(bf16)])
+        held = gathered(held, first_bits)
         return held, layer_out, tokens_grad
 
     kinds = jax.eval_shape(after_forward, products)
@@ -1193,20 +1255,13 @@
     )
 
     out_weight_grad = out_sum.astype(f32)
-    def join(flip, quarter, *waits):
-        return joined(four_place, flip, gate_sum, quarter, results, waits)
-
-    results = []
-    results = join(0, held, out_weight_grad)
-    results = join(1, swapped(held, "wide", 1))
-    near = after(swapped(held, "wide", 2), results[1])
+    core = swapped(held, "wide", 1)
+    (begun,) = joined(four_place, 0, gate_sum, held, core, (), (out_weight_grad,))
+    near = after(swapped(held, "wide", 2), begun)
     far = swapped(near, "wide", 1)
-    results = join(2, near)
-    results = join(3, far)
-    in_weight_grad, small_sum = results
-    conv_at = rank + count + 16
-    gain_at = conv_at + columns + 16
+    conv_at = rank + count + 2
     (
+        in_weight_grad,
         step_weight_grad,
         decay_log_grad,
         skip_gain_grad,
@@ -1215,18 +1270,17 @@
         conv_weight_grad,
         conv_bias_grad,
         norm_gain_grad,
-    ) = small_parts(
-        small_sum,
-        [
-            (0, rank),
-            (rank, count),
-            (rank + count, 1),
-            (rank + count + 1, 1),
-            (conv_at, columns),
-            (conv_at + columns, taps),
-            (conv_at + columns + taps, 1),
-            (gain_at, 1),
-        ],
+    ) = joined(
+        four_place,
+        2,
+        gate_sum,
+        near,
+        far,
+        (begun,),
+        (),
+        (held, core, near, far),
+        (0, rank, rank + count, rank + count + 1, conv_at, conv_at + columns, conv_at + columns + taps),
+        (rank, count, 1, 1, columns, taps, 1, 1),
     )
     return (
         layer_out,

time: 259 us -> 259 us (level)
  waiting for transfers between devices: 76 us -> 83.6 us
  other arithmetic: 15.8 us -> 10.2 us
  local copies, waits for them, and re-layouts: 15.4 us -> 12.7 us
    ppermute x28, waiting for transfers between devices: 68.1 us -> 76.5 us  [swapped(): return lax.ppermute(array, axis, [(i, i ^ bit) for i in range(peers)])]
    slice x5 -> x0, local copies, waits for them, and re-layouts: 5.13 us -> none  [the longest x1 1.85 us: local(): normed = normed_ext[:rows]]
    convert_element_type x2 -> x1, other arithmetic: 3.12 us -> 0.02 us  [after_forward(): spare.astype(bf16)]
    pallas_call x6 -> x4, Pallas kernels: 15.1 us -> 14.8 us  [the longest x2 10.9 us: joined(): pl.pallas_call(functools.partial(join_kernel, small_rows=small_rows), gri...]
    unnamed x44 -> x42, local copies, waits for them, and re-layouts: 5.18 us -> 5.24 us
  transfers between devices with their start and end apart: 34 -> 34, of which waited for: 17 -> 17; matrix products, arithmetic and copies ran while one was open for 13% -> 9% of each run, Pallas kernels for 19% -> 18%
where the time goes in v10:
time: 259 us; the launch traced here: 256 us
  waiting for transfers between devices  83.6 us (32%)
  Pallas kernels  76.1 us (29%)
  starting transfers between devices  42.6 us (16%)
  matrix products  15.7 us (6%)
  between operations  14.9 us (6%)
  local copies, waits for them, and re-layouts  12.7 us (5%)
  other arithmetic  10.2 us (4%)
    ppermute x28, waiting for transfers between devices, swapped(): return lax.ppermute(array, axis, [(i, i ^ bit) for i in range(peers)])  76.5 us
    pallas_call x5, Pallas kernels, call(): pl.pallas_call(kernel, grid=(width // scan_width,), in_specs=in_specs, ou...  50.3 us
    ppermute x28, starting transfers between devices, swapped(): return lax.ppermute(array, axis, [(i, i ^ bit) for i in range(peers)])  30 us
    ppermute x4, starting transfers between devices, passed_along(): return lax.ppermute(array, axis, pairs)  11.2 us
    pallas_call x2, Pallas kernels, joined(): pl.pallas_call(functools.partial(join_kernel, small_rows=small_rows), gri...  10.9 us
    ppermute x4, waiting for transfers between devices, passed_along(): return lax.ppermute(array, axis, pairs)  7.08 us
    unnamed x42, local copies, waits for them, and re-layouts  5.24 us
  transfers between devices with their start and end apart: 34, of which 17 were waited for; matrix products, arithmetic and copies ran while one was open for 9% of the time, Pallas kernels for 18%

profile of v10, /device:TPU:0, one launch (start us, length us, event | category | flops | bytes accessed | tf_op | source)
XLA Modules:
  0.0 256.1 jit_solution(7475363596181683448)
XLA Ops:
  7.2 3.0 %collective-permute-start.21 = (bf16[256,512]{1,0:T(8,128)(2,1)}, bf16[256,512]{1,0:T(8,128)(2,1)S(1)}, u32[]{:S(2)}, u32[]{:S(2)}) collective-permute-start(bf16[256,512]{1,0:T(8,128)(2,1)} %own_ref.1), channel_id=1, source_target_pairs={{0,1},{1,0},{2,3},{3,2},{4,5},{5,4},{6,7},{7,6},{8,9},{9,8},{10,11... | collective-permute-start | bytes 786440 | tf_op jit(solution)/shard_map/ppermute | solution.py:33
  10.3 1.4 edge_rows.1
  11.6 1.3 collective-permute-start.23
  13.0 4.0 %collective-permute-start.22 = (bf16[16,512]{1,0:T(8,128)(2,1)}, bf16[16,512]{1,0:T(8,128)(2,1)S(1)}, u32[]{:S(2)}, u32[]{:S(2)}) collective-permute-start(bf16[16,512]{1,0:T(8,128)(2,1)} %edge_rows.1), channel_id=1, source_target_pairs={{0,2},{2,4},{4,6},{6,8},{8,10},{10,12},{12,14},{14,16},{16,18},{18... | collective-permute-start | bytes 49160 | tf_op jit(solution)/shard_map/ppermute | solution.py:28
  17.0 1.6 collective-permute-start.25
  19.3 2.5 normalized.1
  21.8 4.0 %fusion.25.inner_ref.gate_ref = bf16[2,272,1024]{2,1,0:T(8,128)(2,1)S(1)} fusion(bf16[1024,2,1024]{2,1,0:T(2,128)(2,1)} %param.17, bf16[272,1024]{1,0:T(8,128)(2,1)} %get-tuple-element.151), kind=kOutput, calls=%fused_computation.48 | convolution fusion | flops 1141407744 | bytes 5865472 | tf_op jit(solution)/shard_map/td,dce->cte/dot_general | solution.py:1118
  25.8 3.1 %convolve.1 = (f32[256,1024]{1,0:T(8,128)}, bf16[256,1024]{1,0:T(8,128)(2,1)S(1)}, f32[96,256]{1,0:T(8,128)S(1)}) custom-call(bf16[2,272,1024]{2,1,0:T(8,128)(2,1)S(1)} %fusion.25.inner_ref.gate_ref, f32[4,1024]{1,0:T(4,128)S(1)} %copy-done.32, f32[1,1024]{1,0:T(1,128)} %bitcast.43, bf16[96,1024]{1,0:T(8,128)(2,1)S(1)} %copy-done.16, ...), custom_call_target="tpu_custom_call" | custom-call | flops 1 | bytes 1 | tf_op jit(solution)/shard_map/convolve/pallas_call | solution.py:127
  29.0 0.9 collective-permute-start.24
  30.7 2.9 %collective-permute-done.24.other_ref = f32[96,256]{1,0:T(8,128)S(1)} collective-permute-done((f32[96,256]{1,0:T(8,128)S(1)}, f32[96,256]{1,0:T(8,128)S(1)}, u32[]{:S(2)}, u32[]{:S(2)}) %collective-permute-start.24) | collective-permute-done | bytes 98336 | tf_op jit(solution)/shard_map/ppermute | solution.py:33
  34.2 9.9 %scan_ends.1 = (f32[256,1024]{1,0:T(8,128)}, f32[256,1024]{1,0:T(8,128)}, f32[40,1024]{1,0:T(8,128)}) custom-call(f32[96,256]{1,0:T(8,128)S(1)} %get-tuple-element.153.selected_ref, f32[96,256]{1,0:T(8,128)S(1)} %collective-permute-done.24.other_ref, bf16[64,1024]{1,0:T(8,128)(2,1)S(1)} %copy-done.19, f32[1,1024]{1,0:T(1,128)} %bitcast.44, ...), custom_call_target="tpu_custom_call" | custom-call | flops 1 | bytes 1 | tf_op jit(solution)/shard_map/scan_ends/pallas_call | solution.py:127
  44.2 1.7 collective-permute-done.26.other_ref
  46.6 1.8 carry_round.2
  48.4 1.7 collective-permute-start.27
  50.1 4.9 %collective-permute-done.27.other_ref = f32[40,1024]{1,0:T(8,128)} collective-permute-done((f32[40,1024]{1,0:T(8,128)}, f32[40,1024]{1,0:T(8,128)}, u32[]{:S(2)}, u32[]{:S(2)}) %collective-permute-start.27) | collective-permute-done | bytes 163872 | tf_op jit(solution)/shard_map/ppermute | solution.py:33
  55.0 1.8 carry_round.3
  56.8 4.6 %collective-permute-start.28 = (f32[16,1024]{1,0:T(8,128)}, f32[16,1024]{1,0:T(8,128)S(1)}, u32[]{:S(2)}, u32[]{:S(2)}) collective-permute-start(f32[16,1024]{1,0:T(8,128)} %get-tuple-element.161), channel_id=1, source_target_pairs={{0,8},{2,10},{4,12},{6,14},{8,16},{10,18},{12,20},{14,22},{16,24},... | collective-permute-start | bytes 196616 | tf_op jit(solution)/shard_map/ppermute | solution.py:28
  61.4 1.3 collective-permute-start.29
  62.7 0.9 collective-permute-done.28.entering_ref
  63.6 4.2 %collective-permute-done.29.wait_ref = f32[16,1024]{1,0:T(8,128)S(1)} collective-permute-done((f32[16,1024]{1,0:T(8,128)}, f32[16,1024]{1,0:T(8,128)S(1)}, u32[]{:S(2)}, u32[]{:S(2)}) %collective-permute-start.29) | collective-permute-done | bytes 65568 | tf_op jit(solution)/shard_map/ppermute | solution.py:28
  68.4 9.6 %scan_forward.1 = (bf16[256,1024]{1,0:T(8,128)(2,1)S(1)}, bf16[256,1024]{1,0:T(8,128)(2,1)S(1)}, f32[16,1024]{1,0:T(8,128)}) custom-call(f32[96,256]{1,0:T(8,128)S(1)} %get-tuple-element.153.selected_ref, f32[96,256]{1,0:T(8,128)} %copy-done.15, f32[256,1024]{1,0:T(8,128)} %get-tuple-element.156.step_ref, bf16[256,1024]{1,0:T(8,128)(2,1)S(1)} %get-tuple-element.154.act_ref, ...), custom_call_target="tpu_custom_call" | custom-call | flops 1 | bytes 1 | tf_op jit(solution)/shard_map/scan_forward/pallas_call | solution.py:127
  78.0 2.1 convolution_convert_fusion
  80.1 2.1 convolution_convert_fusion.1
  84.0 137.5 %conditional.1 = (bf16[320,1024]{1,0:T(8,128)(2,1)}, bf16[256,512]{1,0:T(8,128)(2,1)}, bf16[256,512]{1,0:T(8,128)(2,1)}) conditional(s32[]{:T(128)} %bitcast.10, () %tuple.16, (s32[]{:T(128)}, f32[1024]{0:T(1024)S(1)}, f32[96,256]{1,0:T(8,128)S(1)}, f32[96,256]{1,0:T(8,128)}, f32[256,1024]{1,0:T(8,128)}, /*index=5*/f32[256,1024]{1,0:T(8,128)}, ...), branch_computations={%region_0.1_spmd, %region_1.4_spmd} | conditional | flops 1619679488 | bytes 63469256 | solution.py:1250
  85.0 2.5 fusion.32
  87.5 0.9 slice_select_fusion.1
  88.4 1.5 collective-permute-start.1
  89.9 1.8 constant_dynamic-slice_fusion
  92.4 1.4 collective-permute-start.2
  93.8 23.7 %scan_backward.1 = (f32[256,1024]{1,0:T(8,128)}, f32[96,256]{1,0:T(8,128)}, f32[82,1024]{1,0:T(8,128)}) custom-call(f32[96,256]{1,0:T(8,128)S(1)} %get-tuple-element.64.selected_ref, f32[96,256]{1,0:T(8,128)} %get-tuple-element.65.other_ref, f32[256,1024]{1,0:T(8,128)} %get-tuple-element.66.step_pre_ref, f32[256,1024]{1,0:T(8,128)} %get-tuple-element.67.step_ref, ...), custom_call_target="tpu_custom_call" | custom-call | flops 1 | bytes 1 | tf_op jit(solution)/shard_map/cond/branch_1_fun/scan_backward/pallas_call | solution.py:127
  118.1 4.2 %collective-permute-done.other_ref = f32[96,256]{1,0:T(8,128)S(1)} collective-permute-done((f32[96,256]{1,0:T(8,128)}, f32[96,256]{1,0:T(8,128)S(1)}, u32[]{:S(2)}, u32[]{:S(2)}) %collective-permute-start) | collective-permute-done | bytes 98336 | tf_op jit(solution)/shard_map/cond/branch_1_fun/ppermute | solution.py:33
  123.1 4.0 %convolve_grad.1 = (bf16[256,1024]{1,0:T(8,128)(2,1)}, f32[8,1024]{1,0:T(8,128)}, f32[8,1024]{1,0:T(8,128)}, f32[101,1024]{1,0:T(8,128)}) custom-call(f32[96,256]{1,0:T(8,128)} %get-tuple-element.78.select_grad_ref, f32[96,256]{1,0:T(8,128)} %copy-done.30, bf16[96,1024]{1,0:T(8,128)(2,1)S(1)} %copy-done.17, f32[256,1024]{1,0:T(8,128)} %get-tuple-element.80.act_grad_ref, ...), custom_call_target="tpu_custom_call" | custom-call | flops 1 | bytes 1 | tf_op jit(solution)/shard_map/cond/branch_1_fun/convolve_grad/pallas_call | solution.py:127
  127.2 1.3 collective-permute-start.5
  128.5 2.0 collective-permute-done.5.next_ref
  131.1 1.4 patched.1.own_ref
  132.5 1.1 collective-permute-start.6
  133.7 2.1 small_quarters.1
  135.8 2.7 %collective-permute-start.7 = (bf16[64,1024]{1,0:T(8,128)(2,1)}, bf16[64,1024]{1,0:T(8,128)(2,1)S(1)}, u32[]{:S(2)}, u32[]{:S(2)}) collective-permute-start(bf16[64,1024]{1,0:T(8,128)(2,1)} %get-tuple-element.93), channel_id=1, source_target_pairs={{0,2},{2,0},{4,6},{6,4},{8,10},{10,8},{12,14},{14,12},{16,18},{18,... | collective-permute-start | bytes 393224 | tf_op jit(solution)/shard_map/cond/branch_1_fun/ppermute | solution.py:33
  138.9 1.0 collective-permute-start.9
  140.7 10.2 %collective-permute-done.8.refs_2_.second_ref = bf16[64,1024]{1,0:T(8,128)(2,1)S(1)} collective-permute-done((bf16[64,1024]{1,0:T(8,128)(2,1)}, bf16[64,1024]{1,0:T(8,128)(2,1)S(1)}, u32[]{:S(2)}, u32[]{:S(2)}) %collective-permute-start.8) | collective-permute-done | bytes 131104 | tf_op jit(solution)/shard_map/cond/branch_1_fun/ppermute | solution.py:33
  150.9 5.9 %collective-permute-done.9.refs_3_.third_ref = bf16[64,1024]{1,0:T(8,128)(2,1)S(1)} collective-permute-done((bf16[64,1024]{1,0:T(8,128)(2,1)}, bf16[64,1024]{1,0:T(8,128)(2,1)S(1)}, u32[]{:S(2)}, u32[]{:S(2)}) %collective-permute-start.9) | collective-permute-done | bytes 131104 | tf_op jit(solution)/shard_map/cond/branch_1_fun/ppermute | solution.py:33
  158.3 4.4 %fusion.5 = (f32[256]{0:T(256)S(1)}, f32[1024]{0:T(1024)S(1)}, f32[256,1024]{1,0:T(8,128)S(1)}) fusion(bf16[256,1024]{1,0:T(8,128)(2,1)} %get-tuple-element.100, f32[1024]{0:T(1024)S(1)} %get-tuple-element.99, f32[256]{0:T(256)S(1)} %bitcast.41, bf16[1024,2,1024]{2,1,0:T(2,128)(2,1)} %get-tuple-element.207, bf16[1,256,1024]{2,1,0:T(8,128)(2,1)} %bitcast.36, ...), kind=kOutput, calls=%fused_computation.5 | convolution fusion | flops 1076099840 | bytes 6825984 | tf_op jit(solution)/shard_map/cond/branch_1_fun/cte,dce->td/dot_general | solution.py:1207
  163.3 1.5 collective-permute-start.16
  167.1 3.8 %inner_quarter.1 = (f32[80,1024]{1,0:T(8,128)}, bf16[80,1024]{1,0:T(8,128)(2,1)}, bf16[80,1024]{1,0:T(8,128)(2,1)}, bf16[80,1024]{1,0:T(8,128)(2,1)}) custom-call(s32[1]{0:T(128)} %bitcast.place_ref, bf16[256,1024]{1,0:T(8,128)(2,1)} %patched.1.own_ref, bf16[256,1024]{1,0:T(8,128)(2,1)} %after.2.near_ref, bf16[256,1024]{1,0:T(8,128)(2,1)} %collective-permute-done.10.far_ref, ...), custom_call_target="tpu_custom_call" | custom-call | flops 1 | bytes 1 | tf_op jit(solution)/shard_map/cond/branch_1_fun/inner_quarter/pallas_call | solution.py:939
  170.9 2.2 collective-permute-start.13
  173.1 1.0 collective-permute-start.14
  174.2 1.4 collective-permute-start.15
  176.3 8.3 %collective-permute-done.13 = bf16[80,1024]{1,0:T(8,128)(2,1)S(1)} collective-permute-done((bf16[80,1024]{1,0:T(8,128)(2,1)}, bf16[80,1024]{1,0:T(8,128)(2,1)S(1)}, u32[]{:S(2)}, u32[]{:S(2)}) %collective-permute-start.13) | collective-permute-done | bytes 163872 | tf_op jit(solution)/shard_map/cond/branch_1_fun/ppermute | solution.py:33
  184.6 3.1 %collective-permute-done.14 = bf16[80,1024]{1,0:T(8,128)(2,1)S(1)} collective-permute-done((bf16[80,1024]{1,0:T(8,128)(2,1)}, bf16[80,1024]{1,0:T(8,128)(2,1)S(1)}, u32[]{:S(2)}, u32[]{:S(2)}) %collective-permute-start.14) | collective-permute-done | bytes 163872 | tf_op jit(solution)/shard_map/cond/branch_1_fun/ppermute | solution.py:33
  187.6 10.1 %collective-permute-done.15 = bf16[80,1024]{1,0:T(8,128)(2,1)S(1)} collective-permute-done((bf16[80,1024]{1,0:T(8,128)(2,1)}, bf16[80,1024]{1,0:T(8,128)(2,1)S(1)}, u32[]{:S(2)}, u32[]{:S(2)}) %collective-permute-start.15) | collective-permute-done | bytes 163872 | tf_op jit(solution)/shard_map/cond/branch_1_fun/ppermute | solution.py:33
  197.7 1.1 fusion.18
  198.8 1.1 collective-permute-start.19
  199.9 2.1 fusion.15
  201.9 1.0 collective-permute-start.18
  203.0 2.4 collective-permute-start.17
  205.3 5.6 %collective-permute-done.19 = bf16[80,1024]{1,0:T(8,128)(2,1)S(1)} collective-permute-done((bf16[80,1024]{1,0:T(8,128)(2,1)S(1)}, bf16[80,1024]{1,0:T(8,128)(2,1)S(1)}, u32[]{:S(2)}, u32[]{:S(2)}) %collective-permute-start.19) | collective-permute-done | bytes 163872 | tf_op jit(solution)/shard_map/cond/branch_1_fun/ppermute | solution.py:33
  211.1 9.3 %collective-permute-done.18 = bf16[80,1024]{1,0:T(8,128)(2,1)S(1)} collective-permute-done((bf16[80,1024]{1,0:T(8,128)(2,1)S(1)}, bf16[80,1024]{1,0:T(8,128)(2,1)S(1)}, u32[]{:S(2)}, u32[]{:S(2)}) %collective-permute-start.18) | collective-permute-done | bytes 163872 | tf_op jit(solution)/shard_map/cond/branch_1_fun/ppermute | solution.py:33
  220.6 1.0 pad_maximum_fusion
  222.3 4.1 %convert_element_type.61.rest_0_ = f32[1024,1024]{1,0:T(8,128)} convert(bf16[1024,1024]{1,0:T(8,128)(2,1)} %get-tuple-element.216) | non-fusion elementwise | flops 1048576 | bytes 6291456 | tf_op jit(solution)/shard_map/convert_element_type | solution.py:1257
  227.2 4.6 %joined.2.refs_1_.rest_4_ = f32[1024,2,1024]{2,1,0:T(2,128)} custom-call(s32[1]{0:T(128)} %bitcast.20.place_ref, bf16[1024,1024]{1,0:T(8,128)(2,1)} %get-tuple-element.215.gate_ref, bf16[320,1024]{1,0:T(8,128)(2,1)} %get-tuple-element.172.first_ref.rest_0_, bf16[320,1024]{1,0:T(8,128)(2,1)} %copy-done.4, f32[1024,1024]{1,0:T(8,128)} %convert_element_type.61.rest_0_), custom_call_target="tpu_custom_call" | custom-call | flops 1 | bytes 1 | tf_op jit(solution)/shard_map/joined/pallas_call | solution.py:1004
  231.8 7.1 %collective-permute-done.30.refs_0_ = bf16[320,1024]{1,0:T(8,128)(2,1)S(1)} collective-permute-done((bf16[320,1024]{1,0:T(8,128)(2,1)}, bf16[320,1024]{1,0:T(8,128)(2,1)S(1)}, u32[]{:S(2)}, u32[]{:S(2)}) %collective-permute-start.30) | collective-permute-done | bytes 655392 | tf_op jit(solution)/shard_map/ppermute | solution.py:33
  238.9 0.9 copy-done.3
  239.8 2.3 collective-permute-done.32.second_ref.rest_3_
  242.9 6.3 %joined.3 = (f32[1024,2,1024]{2,1,0:T(2,128)}, f32[64,1024]{1,0:T(8,128)}, f32[16,1024]{1,0:T(8,128)}, f32[1,1024]{1,0:T(1,128)}, f32[1,1024]{1,0:T(1,128)}, /*i...) custom-call(s32[1]{0:T(128)} %bitcast.20.place_ref, ...), custom_call_target="tpu_custom_call", output_to_operand_aliasing={{0}: (8, {})} | custom-call | flops 1 | bytes 1 | tf_op jit(solution)/shard_map/joined/pallas_call | solution.py:1004
  (128 shorter events, 17.4 us)
Async XLA Ops:
  7.2 215.1 %all-reduce.3.cloned.1.call-start = ((), (), s32[]{:S(2)}) async-start(), calls=%async_computation | async-start | bytes 8388608 | tf_op jit(solution)/shard_map/psum | solution.py:1159
  7.2 11.4 %collective-permute-start.21 = (bf16[256,512]{1,0:T(8,128)(2,1)}, bf16[256,512]{1,0:T(8,128)(2,1)S(1)}, u32[]{:S(2)}, u32[]{:S(2)}) collective-permute-start(bf16[256,512]{1,0:T(8,128)(2,1)} %own_ref.1), channel_id=1, source_target_pairs={{0,1},{1,0},{2,3},{3,2},{4,5},{5,4},{6,7},{7,6},{8,9},{9,8},{10,11... | collective-permute-start | bytes 786440 | tf_op jit(solution)/shard_map/ppermute | solution.py:33
  11.6 7.0 %collective-permute-start.23 = (bf16[16,512]{1,0:T(8,128)(2,1)}, bf16[16,512]{1,0:T(8,128)(2,1)S(1)}, u32[]{:S(2)}, u32[]{:S(2)}) collective-permute-start(bf16[16,512]{1,0:T(8,128)(2,1)} %edge_rows.1), channel_id=1, source_target_pairs={{0,3},{1,2},{2,5},{3,4},{4,7},{5,6},{6,9},{7,8},{8,11},{9,10},{10,... | collective-permute-start | bytes 49160 | tf_op jit(solution)/shard_map/ppermute | solution.py:51
  13.0 5.6 %collective-permute-start.22 = (bf16[16,512]{1,0:T(8,128)(2,1)}, bf16[16,512]{1,0:T(8,128)(2,1)S(1)}, u32[]{:S(2)}, u32[]{:S(2)}) collective-permute-start(bf16[16,512]{1,0:T(8,128)(2,1)} %edge_rows.1), channel_id=1, source_target_pairs={{0,2},{2,4},{4,6},{6,8},{8,10},{10,12},{12,14},{14,16},{16,18},{18... | collective-permute-start | bytes 49160 | tf_op jit(solution)/shard_map/ppermute | solution.py:28
  17.0 12.9 %collective-permute-start.25 = (bf16[256,512]{1,0:T(8,128)(2,1)}, bf16[256,512]{1,0:T(8,128)(2,1)S(1)}, u32[]{:S(2)}, u32[]{:S(2)}) collective-permute-start(bf16[256,512]{1,0:T(8,128)(2,1)} %param.27), channel_id=1, source_target_pairs={{0,1},{1,0},{2,3},{3,2},{4,5},{5,4},{6,7},{7,6},{8,9},{9,8},{10,11... | collective-permute-start | bytes 786440 | tf_op jit(solution)/shard_map/ppermute | solution.py:33
  18.6 0.7 copy-start.28
  21.8 4.0 %copy-start.16 = (bf16[96,1024]{1,0:T(8,128)(2,1)S(1)}, bf16[96,1024]{1,0:T(8,128)(2,1)}, u32[]{:S(2)}) copy-start(bf16[96,1024]{1,0:T(8,128)(2,1)} %select_ref.1) | copy-start | bytes 589828
  21.8 4.0 %copy-start.32 = (f32[4,1024]{1,0:T(4,128)S(1)}, f32[4,1024]{1,0:T(4,128)}, u32[]{:S(2)}) copy-start(f32[4,1024]{1,0:T(4,128)} %conv_weight_ref.1) | copy-start | bytes 49156
  21.8 8.1 %copy-start.12 = (bf16[256,512]{1,0:T(8,128)(2,1)S(1)}, bf16[256,512]{1,0:T(8,128)(2,1)}, u32[]{:S(2)}) copy-start(bf16[256,512]{1,0:T(8,128)(2,1)} %param.27) | copy-start | bytes 786436
  25.8 4.2 %copy-start = (bf16[1024,1024]{1,0:T(8,128)(2,1)S(1)}, bf16[1024,1024]{1,0:T(8,128)(2,1)}, u32[]{:S(2)}) copy-start(bf16[1024,1024]{1,0:T(8,128)(2,1)} %param.25) | copy-start | bytes 6291460
  29.0 4.6 %collective-permute-start.24 = (f32[96,256]{1,0:T(8,128)S(1)}, f32[96,256]{1,0:T(8,128)S(1)}, u32[]{:S(2)}, u32[]{:S(2)}) collective-permute-start(f32[96,256]{1,0:T(8,128)S(1)} %get-tuple-element.153.selected_ref), channel_id=1, source_target_pairs={{0,1},{1,0},{2,3},{3,2},{4,5},{5,4},{6,7},{7,6},{8,9},{9,8},{10,11... | collective-permute-start | bytes 294920 | tf_op jit(solution)/shard_map/ppermute | solution.py:33
  30.0 4.3 %copy-start.11 = (f32[16,1024]{1,0:T(8,128)S(1)}, f32[16,1024]{1,0:T(8,128)}, u32[]{:S(2)}) copy-start(f32[16,1024]{1,0:T(8,128)} %decay_log_ref.7) | copy-start | bytes 196612
  30.0 4.3 %copy-start.19 = (bf16[64,1024]{1,0:T(8,128)(2,1)S(1)}, bf16[64,1024]{1,0:T(8,128)(2,1)}, u32[]{:S(2)}) copy-start(bf16[64,1024]{1,0:T(8,128)(2,1)} %step_weight_ref.1) | copy-start | bytes 393220
  34.2 34.2 %copy-start.34 = (f32[1024]{0:T(1024)S(1)}, f32[1024]{0:T(1024)}, u32[]{:S(2)}) copy-start(f32[1024]{0:T(1024)} %param.24) | copy-start | bytes 12292
  44.2 1.7 collective-permute-start.26
  48.4 6.6 %collective-permute-start.27 = (f32[40,1024]{1,0:T(8,128)}, f32[40,1024]{1,0:T(8,128)}, u32[]{:S(2)}, u32[]{:S(2)}) collective-permute-start(f32[40,1024]{1,0:T(8,128)} %get-tuple-element.158.own_ref), channel_id=1, source_target_pairs={{0,4},{2,6},{4,0},{6,2},{8,12},{10,14},{12,8},{14,10},{16,20},{18,... | collective-permute-start | bytes 491528 | tf_op jit(solution)/shard_map/ppermute | solution.py:33
  56.8 6.8 %collective-permute-start.28 = (f32[16,1024]{1,0:T(8,128)}, f32[16,1024]{1,0:T(8,128)S(1)}, u32[]{:S(2)}, u32[]{:S(2)}) collective-permute-start(f32[16,1024]{1,0:T(8,128)} %get-tuple-element.161), channel_id=1, source_target_pairs={{0,8},{2,10},{4,12},{6,14},{8,16},{10,18},{12,20},{14,22},{16,24},... | collective-permute-start | bytes 196616 | tf_op jit(solution)/shard_map/ppermute | solution.py:28
  61.4 6.4 %collective-permute-start.29 = (f32[16,1024]{1,0:T(8,128)}, f32[16,1024]{1,0:T(8,128)S(1)}, u32[]{:S(2)}, u32[]{:S(2)}) collective-permute-start(f32[16,1024]{1,0:T(8,128)} %get-tuple-element.162), channel_id=1, source_target_pairs={{8,0},{10,2},{12,4},{14,6},{16,8},{18,10},{20,12},{22,14},{24,16},... | collective-permute-start | bytes 196616 | tf_op jit(solution)/shard_map/ppermute | solution.py:28
  63.6 4.2 %copy-start.31 = (f32[16,1024]{1,0:T(8,128)}, f32[16,1024]{1,0:T(8,128)S(1)}, u32[]{:S(2)}) copy-start(f32[16,1024]{1,0:T(8,128)S(1)} %collective-permute-done.28.entering_ref) | copy-start | bytes 196612
  78.0 2.1 copy-start.8
  78.0 2.1 copy-start.20
  78.0 2.1 copy-start.10
  82.2 1.8 copy-start.35
  84.2 0.8 copy-start.1
  88.4 33.9 %collective-permute-start.1 = (f32[256,512]{1,0:T(8,128)}, f32[256,512]{1,0:T(8,128)}, u32[]{:S(2)}, u32[]{:S(2)}) collective-permute-start(f32[256,512]{1,0:T(8,128)} %slice_select_fusion.1), channel_id=1, source_target_pairs={{0,1},{1,0},{2,3},{3,2},{4,5},{5,4},{6,7},{7,6},{8,9},{9,8},{10,11... | collective-permute-start | bytes 1572872 | tf_op jit(solution)/shard_map/cond/branch_1_fun/ppermute | solution.py:33
  91.7 30.7 %collective-permute-start.4 = (bf16[256,256]{1,0:T(8,128)(2,1)S(1)}, bf16[256,256]{1,0:T(8,128)(2,1)S(1)}, u32[]{:S(2)}, u32[]{:S(2)}) collective-permute-start(bf16[256,256]{1,0:T(8,128)(2,1)S(1)} %get-tuple-element.219), channel_id=1, source_target_pairs={{0,6},{2,4},{4,2},{6,0},{8,14},{10,12},{12,10},{14,8},{16,22},{18,... | collective-permute-start | bytes 393224 | tf_op jit(solution)/shard_map/cond/branch_1_fun/ppermute | solution.py:33
  91.7 30.7 %collective-permute-start.3 = (bf16[256,256]{1,0:T(8,128)(2,1)S(1)}, bf16[256,256]{1,0:T(8,128)(2,1)S(1)}, u32[]{:S(2)}, u32[]{:S(2)}) collective-permute-start(bf16[256,256]{1,0:T(8,128)(2,1)S(1)} %get-tuple-element.220), channel_id=1, source_target_pairs={{0,2},{2,0},{4,6},{6,4},{8,10},{10,8},{12,14},{14,12},{16,18},{18,... | collective-permute-start | bytes 393224 | tf_op jit(solution)/shard_map/cond/branch_1_fun/ppermute | solution.py:33
  92.4 30.0 %collective-permute-start.2 = (bf16[256,256]{1,0:T(8,128)(2,1)S(1)}, bf16[256,256]{1,0:T(8,128)(2,1)S(1)}, u32[]{:S(2)}, u32[]{:S(2)}) collective-permute-start(bf16[256,256]{1,0:T(8,128)(2,1)S(1)} %get-tuple-element.221), channel_id=1, source_target_pairs={{0,4},{2,6},{4,0},{6,2},{8,12},{10,14},{12,8},{14,10},{16,20},{18,... | collective-permute-start | bytes 393224 | tf_op jit(solution)/shard_map/cond/branch_1_fun/ppermute | solution.py:33
  93.8 29.3 %copy-start.2 = (bf16[256,1024]{1,0:T(8,128)(2,1)S(1)}, bf16[256,1024]{1,0:T(8,128)(2,1)}, u32[]{:S(2)}) copy-start(bf16[256,1024]{1,0:T(8,128)(2,1)} %copy-done.1) | copy-start | bytes 1572868 | tf_op jit(solution)/shard_map/cond
  93.8 29.3 %copy-start.14 = (f32[256,1024]{1,0:T(8,128)S(1)}, f32[256,1024]{1,0:T(8,128)}, u32[]{:S(2)}) copy-start(f32[256,1024]{1,0:T(8,128)} %get-tuple-element.81.convolved_ref) | copy-start | bytes 3145732 | tf_op jit(solution)/shard_map/cond
  93.8 29.3 %copy-start.17 = (bf16[96,1024]{1,0:T(8,128)(2,1)S(1)}, bf16[96,1024]{1,0:T(8,128)(2,1)}, u32[]{:S(2)}) copy-start(bf16[96,1024]{1,0:T(8,128)(2,1)} %get-tuple-element.79.select_ref) | copy-start | bytes 589828 | tf_op jit(solution)/shard_map/cond
  117.5 4.9 %collective-permute-start = (f32[96,256]{1,0:T(8,128)}, f32[96,256]{1,0:T(8,128)S(1)}, u32[]{:S(2)}, u32[]{:S(2)}) collective-permute-start(f32[96,256]{1,0:T(8,128)} %get-tuple-element.78.select_grad_ref), channel_id=1, source_target_pairs={{0,1},{1,0},{2,3},{3,2},{4,5},{5,4},{6,7},{7,6},{8,9},{9,8},{10,11... | collective-permute-start | bytes 294920 | tf_op jit(solution)/shard_map/cond/branch_1_fun/ppermute | solution.py:33
  122.4 0.7 copy-start.25
  122.4 0.7 copy-start.26
  123.1 10.5 %copy-start.29 = (f32[256,1]{1,0:T(8,128)S(1)}, f32[256,1]{1,0:T(8,128)}, u32[]{:S(2)}) copy-start(f32[256,1]{1,0:T(8,128)} %get-tuple-element.210) | copy-start | bytes 3076 | tf_op jit(solution)/shard_map/cond
  127.2 3.3 %collective-permute-start.5 = (f32[8,1024]{1,0:T(8,128)}, f32[8,1024]{1,0:T(8,128)S(1)}, u32[]{:S(2)}, u32[]{:S(2)}) collective-permute-start(f32[8,1024]{1,0:T(8,128)} %get-tuple-element.89), channel_id=1, source_target_pairs={{2,0},{4,2},{6,4},{8,6},{10,8},{12,10},{14,12},{16,14},{18,16},{20... | collective-permute-start | bytes 98312 | tf_op jit(solution)/shard_map/cond/branch_1_fun/ppermute | solution.py:28
  132.5 25.8 %copy-start.7 = (bf16[256,1024]{1,0:T(8,128)(2,1)S(1)}, bf16[256,1024]{1,0:T(8,128)(2,1)}, u32[]{:S(2)}) copy-start(bf16[256,1024]{1,0:T(8,128)(2,1)} %patched.1.own_ref) | copy-start | bytes 1572868 | tf_op jit(solution)/shard_map/cond
  132.5 24.3 %collective-permute-start.6 = (bf16[256,1024]{1,0:T(8,128)(2,1)}, bf16[256,1024]{1,0:T(8,128)(2,1)S(1)}, u32[]{:S(2)}, u32[]{:S(2)}) collective-permute-start(bf16[256,1024]{1,0:T(8,128)(2,1)} %patched.1.own_ref), channel_id=1, source_target_pairs={{0,4},{2,6},{4,0},{6,2},{8,12},{10,14},{12,8},{14,10},{16,20},{18,... | collective-permute-start | bytes 1572872 | tf_op jit(solution)/shard_map/cond/branch_1_fun/ppermute | solution.py:33
  135.8 4.9 %collective-permute-start.7 = (bf16[64,1024]{1,0:T(8,128)(2,1)}, bf16[64,1024]{1,0:T(8,128)(2,1)S(1)}, u32[]{:S(2)}, u32[]{:S(2)}) collective-permute-start(bf16[64,1024]{1,0:T(8,128)(2,1)} %get-tuple-element.93), channel_id=1, source_target_pairs={{0,2},{2,0},{4,6},{6,4},{8,10},{10,8},{12,14},{14,12},{16,18},{18,... | collective-permute-start | bytes 393224 | tf_op jit(solution)/shard_map/cond/branch_1_fun/ppermute | solution.py:33
  138.6 12.3 %collective-permute-start.8 = (bf16[64,1024]{1,0:T(8,128)(2,1)}, bf16[64,1024]{1,0:T(8,128)(2,1)S(1)}, u32[]{:S(2)}, u32[]{:S(2)}) collective-permute-start(bf16[64,1024]{1,0:T(8,128)(2,1)} %get-tuple-element.94), channel_id=1, source_target_pairs={{0,4},{2,6},{4,0},{6,2},{8,12},{10,14},{12,8},{14,10},{16,20},{18,... | collective-permute-start | bytes 393224 | tf_op jit(solution)/shard_map/cond/branch_1_fun/ppermute | solution.py:33
  138.9 17.9 %collective-permute-start.9 = (bf16[64,1024]{1,0:T(8,128)(2,1)}, bf16[64,1024]{1,0:T(8,128)(2,1)S(1)}, u32[]{:S(2)}, u32[]{:S(2)}) collective-permute-start(bf16[64,1024]{1,0:T(8,128)(2,1)} %get-tuple-element.95), channel_id=1, source_target_pairs={{0,6},{2,4},{4,2},{6,0},{8,14},{10,12},{12,10},{14,8},{16,22},{18,... | collective-permute-start | bytes 393224 | tf_op jit(solution)/shard_map/cond/branch_1_fun/ppermute | solution.py:33
  139.9 26.4 %collective-permute-start.10 = (bf16[256,1024]{1,0:T(8,128)(2,1)}, bf16[256,1024]{1,0:T(8,128)(2,1)}, u32[]{:S(2)}, u32[]{:S(2)}) collective-permute-start(bf16[256,1024]{1,0:T(8,128)(2,1)} %patched.1.own_ref), channel_id=1, source_target_pairs={{0,2},{2,0},{4,6},{6,4},{8,10},{10,8},{12,14},{14,12},{16,18},{18,... | collective-permute-start | bytes 1572872 | tf_op jit(solution)/shard_map/cond/branch_1_fun/ppermute | solution.py:33
  140.7 16.1 %copy-start.21 = (bf16[64,1024]{1,0:T(8,128)(2,1)}, bf16[64,1024]{1,0:T(8,128)(2,1)S(1)}, u32[]{:S(2)}) copy-start(bf16[64,1024]{1,0:T(8,128)(2,1)S(1)} %collective-permute-done.7.refs_1_.first_ref) | copy-start | bytes 393220 | tf_op jit(solution)/shard_map/cond
  150.9 5.9 %copy-start.22 = (bf16[64,1024]{1,0:T(8,128)(2,1)}, bf16[64,1024]{1,0:T(8,128)(2,1)S(1)}, u32[]{:S(2)}) copy-start(bf16[64,1024]{1,0:T(8,128)(2,1)S(1)} %collective-permute-done.8.refs_2_.second_ref) | copy-start | bytes 393220 | tf_op jit(solution)/shard_map/cond
  157.5 0.9 copy-start.9
  158.3 8.0 %collective-permute-start.11 = (bf16[256,1024]{1,0:T(8,128)(2,1)}, bf16[256,1024]{1,0:T(8,128)(2,1)S(1)}, u32[]{:S(2)}, u32[]{:S(2)}) collective-permute-start(bf16[256,1024]{1,0:T(8,128)(2,1)} %after.2.near_ref), channel_id=1, source_target_pairs={{0,2},{2,0},{4,6},{6,4},{8,10},{10,8},{12,14},{14,12},{16,18},{18,... | collective-permute-start | bytes 1572872 | tf_op jit(solution)/shard_map/cond/branch_1_fun/ppermute | solution.py:33
  162.7 3.6 %collective-permute-start.12 = (f32[1,256]{1,0:T(1,128)S(1)}, f32[1,256]{1,0:T(1,128)S(1)}, u32[]{:S(2)}, u32[]{:S(2)}) collective-permute-start(f32[1,256]{1,0:T(1,128)S(1)} %bitcast.49), channel_id=1, source_target_pairs={{0,1},{1,0},{2,3},{3,2},{4,5},{5,4},{6,7},{7,6},{8,9},{9,8},{10,11... | collective-permute-start | bytes 3080 | tf_op jit(solution)/shard_map/cond/branch_1_fun/ppermute | solution.py:33
  163.3 12.9 %collective-permute-start.16 = (f32[1,1024]{1,0:T(1,128)S(1)}, f32[1,1024]{1,0:T(1,128)S(1)}, u32[]{:S(2)}, u32[]{:S(2)}) collective-permute-start(f32[1,1024]{1,0:T(1,128)S(1)} %bitcast.45), channel_id=1, source_target_pairs={{0,1},{1,0},{2,3},{3,2},{4,5},{5,4},{6,7},{7,6},{8,9},{9,8},{10,11... | collective-permute-start | bytes 12296 | tf_op jit(solution)/shard_map/cond/branch_1_fun/ppermute | solution.py:33
  164.9 35.0 %collective-permute-start.20 = (f32[256,512]{1,0:T(8,128)S(1)}, f32[256,512]{1,0:T(8,128)S(1)}, u32[]{:S(2)}, u32[]{:S(2)}) collective-permute-start(f32[256,512]{1,0:T(8,128)S(1)} %slice_select_fusion), channel_id=1, source_target_pairs={{0,1},{1,0},{2,3},{3,2},{4,5},{5,4},{6,7},{7,6},{8,9},{9,8},{10,11... | collective-permute-start | bytes 1572872 | tf_op jit(solution)/shard_map/cond/branch_1_fun/ppermute | solution.py:33
  166.3 0.8 copy-start.18
  167.1 32.7 %copy-start.6 = (bf16[256,512]{1,0:T(8,128)(2,1)S(1)}, bf16[256,512]{1,0:T(8,128)(2,1)}, u32[]{:S(2)}) copy-start(bf16[256,512]{1,0:T(8,128)(2,1)} %get-tuple-element.106) | copy-start | bytes 786436 | tf_op jit(solution)/shard_map/cond
  167.1 32.7 %copy-start.13 = (bf16[256,512]{1,0:T(8,128)(2,1)S(1)}, bf16[256,512]{1,0:T(8,128)(2,1)}, u32[]{:S(2)}) copy-start(bf16[256,512]{1,0:T(8,128)(2,1)} %get-tuple-element.107) | copy-start | bytes 786436 | tf_op jit(solution)/shard_map/cond
  170.9 13.7 %collective-permute-start.13 = (bf16[80,1024]{1,0:T(8,128)(2,1)}, bf16[80,1024]{1,0:T(8,128)(2,1)S(1)}, u32[]{:S(2)}, u32[]{:S(2)}) collective-permute-start(bf16[80,1024]{1,0:T(8,128)(2,1)} %get-tuple-element.102), channel_id=1, source_target_pairs={{0,8},{2,10},{4,12},{6,14},{8,0},{10,2},{12,4},{14,6},{16,24},{18,... | collective-permute-start | bytes 491528 | tf_op jit(solution)/shard_map/cond/branch_1_fun/ppermute | solution.py:33
  173.1 14.5 %collective-permute-start.14 = (bf16[80,1024]{1,0:T(8,128)(2,1)}, bf16[80,1024]{1,0:T(8,128)(2,1)S(1)}, u32[]{:S(2)}, u32[]{:S(2)}) collective-permute-start(bf16[80,1024]{1,0:T(8,128)(2,1)} %get-tuple-element.103), channel_id=1, source_target_pairs={{0,16},{2,18},{4,20},{6,22},{8,24},{10,26},{12,28},{14,30},{16,0},... | collective-permute-start | bytes 491528 | tf_op jit(solution)/shard_map/cond/branch_1_fun/ppermute | solution.py:33
  174.2 23.5 %collective-permute-start.15 = (bf16[80,1024]{1,0:T(8,128)(2,1)}, bf16[80,1024]{1,0:T(8,128)(2,1)S(1)}, u32[]{:S(2)}, u32[]{:S(2)}) collective-permute-start(bf16[80,1024]{1,0:T(8,128)(2,1)} %get-tuple-element.104), channel_id=1, source_target_pairs={{0,24},{2,26},{4,28},{6,30},{8,16},{10,18},{12,20},{14,22},{16,8},... | collective-permute-start | bytes 491528 | tf_op jit(solution)/shard_map/cond/branch_1_fun/ppermute | solution.py:33
  198.8 12.2 %collective-permute-start.19 = (bf16[80,1024]{1,0:T(8,128)(2,1)S(1)}, bf16[80,1024]{1,0:T(8,128)(2,1)S(1)}, u32[]{:S(2)}, u32[]{:S(2)}) collective-permute-start(bf16[80,1024]{1,0:T(8,128)(2,1)S(1)} %pad_maximum_fusion.3), channel_id=1, source_target_pairs={{0,8},{2,10},{4,12},{6,14},{8,0},{10,2},{12,4},{14,6},{16,24},{18,... | collective-permute-start | bytes 491528 | tf_op jit(solution)/shard_map/cond/branch_1_fun/ppermute | solution.py:33
  201.9 18.4 %collective-permute-start.18 = (bf16[80,1024]{1,0:T(8,128)(2,1)S(1)}, bf16[80,1024]{1,0:T(8,128)(2,1)S(1)}, u32[]{:S(2)}, u32[]{:S(2)}) collective-permute-start(bf16[80,1024]{1,0:T(8,128)(2,1)S(1)} %pad_maximum_fusion.3), channel_id=1, source_target_pairs={{0,16},{2,18},{4,20},{6,22},{8,24},{10,26},{12,28},{14,30},{16,0},... | collective-permute-start | bytes 491528 | tf_op jit(solution)/shard_map/cond/branch_1_fun/ppermute | solution.py:33
  203.0 17.4 %collective-permute-start.17 = (bf16[80,1024]{1,0:T(8,128)(2,1)S(1)}, bf16[80,1024]{1,0:T(8,128)(2,1)S(1)}, u32[]{:S(2)}, u32[]{:S(2)}) collective-permute-start(bf16[80,1024]{1,0:T(8,128)(2,1)S(1)} %pad_maximum_fusion.3), channel_id=1, source_target_pairs={{0,24},{2,26},{4,28},{6,30},{8,16},{10,18},{12,20},{14,22},{16,8},... | collective-permute-start | bytes 491528 | tf_op jit(solution)/shard_map/cond/branch_1_fun/ppermute | solution.py:33
  221.5 4.8 %collective-permute-start.31 = (bf16[320,1024]{1,0:T(8,128)(2,1)}, bf16[320,1024]{1,0:T(8,128)(2,1)S(1)}, u32[]{:S(2)}, u32[]{:S(2)}) collective-permute-start(bf16[320,1024]{1,0:T(8,128)(2,1)} %get-tuple-element.172.first_ref.rest_0_), channel_id=1, source_target_pairs={{0,2},{2,0},{4,6},{6,4},{8,10},{10,8},{12,14},{14,12},{16,18},{18,... | collective-permute-start | bytes 1966088 | tf_op jit(solution)/shard_map/ppermute | solution.py:33
  221.6 17.4 %collective-permute-start.30 = (bf16[320,1024]{1,0:T(8,128)(2,1)}, bf16[320,1024]{1,0:T(8,128)(2,1)S(1)}, u32[]{:S(2)}, u32[]{:S(2)}) collective-permute-start(bf16[320,1024]{1,0:T(8,128)(2,1)} %get-tuple-element.172.first_ref.rest_0_), channel_id=1, source_target_pairs={{0,4},{2,6},{4,0},{6,2},{8,12},{10,14},{12,8},{14,10},{16,20},{18,... | collective-permute-start | bytes 1966088 | tf_op jit(solution)/shard_map/ppermute | solution.py:33
  226.4 0.9 copy-start.4
  238.9 0.9 copy-start.3
  239.8 2.3 collective-permute-start.32
  242.1 0.8 copy-start.5
  (10 other events, 6.3 us)
Sparse Core Ops, SparseCore 0:
  82.3 138.2 all-reduce.2

commit v11 on v10

--- a/solution.py
+++ b/solution.py
@@ -81,8 +81,10 @@
     return total
 
 
-def gathered(held, bits):
+def gathered(held, bits, *waits):
     blocks = [held] + [swapped(held, "wide", flip) for flip in flips(bits)[1:]]
+    if waits:
+        blocks[1] = after(blocks[1], *waits)
     for bit in bits:
         upper = is_upper(bit)
         blocks = [
@@ -90,6 +92,32 @@
             for a, b in zip(blocks[0::2], blocks[1::2])
         ]
     return blocks[0]
+
+
+def halves_of(array, axis):
+    upper = is_upper(1).astype(jnp.int32)
+    half = array.shape[axis] // 2
+    return (
+        lax.dynamic_slice_in_dim(array, upper * half, half, axis),
+        lax.dynamic_slice_in_dim(array, (1 - upper) * half, half, axis),
+    )
+
+
+def folded(keep, arrived, bit):
+    half = keep.shape[0] // 2
+    upper = is_upper(bit).astype(jnp.int32)
+
+    def rows(start):
+        return lax.dynamic_slice_in_dim(keep, start, half, 0) + lax.dynamic_slice_in_dim(
+            arrived, start, half, 0
+        ).astype(f32)
+
+    return rows(upper * half), rows((1 - upper) * half).astype(bf16)
+
+
+def unfolded(held, arrived, bit):
+    upper = is_upper(bit)
+    return jnp.concatenate([jnp.where(upper, arrived, held), jnp.where(upper, held, arrived)])
 
 
 def quarter_of_four(array):
@@ -356,7 +384,6 @@
     passed_ref,
     entering_ref,
     skip_ref,
-    wait_ref,
     gated_ref,
     gate_grad_ref,
     entry_ref,
@@ -399,7 +426,7 @@
 
 
 def scan_forward(
-    selected, other, step, act, projected, gated_grad, masks, decay_log, passed, entering, skip_gain, wait
+    selected, other, step, act, projected, gated_grad, masks, decay_log, passed, entering, skip_gain
 ):
     rows, width = step.shape
     count = decay_log.shape[0]
@@ -420,7 +447,6 @@
             column_spec(2 * count + 8),
             column_spec(count),
             column_spec(1),
-            pl.BlockSpec(memory_space=pl.ANY),
         ],
         [column_spec(rows), column_spec(rows), column_spec(count)],
         [
@@ -442,7 +468,6 @@
         passed,
         entering,
         skip_gain,
-        wait,
     )
 
 
@@ -461,6 +486,7 @@
     returning_ref,
     skip_ref,
     step_weight_ref,
+    wait_ref,
     act_grad_ref,
     select_grad_ref,
     small_ref,
@@ -575,6 +601,7 @@
     returning,
     skip_gain,
     step_weight,
+    wait,
 ):
     rows, width = step.shape
     count = decay_log.shape[0]
@@ -601,6 +628,7 @@
             column_spec(count),
             column_spec(1),
             column_spec(rank),
+            pl.BlockSpec(memory_space=pl.ANY),
         ],
         [column_spec(rows), whole_spec(columns, rows), column_spec(small)],
         [
@@ -632,6 +660,7 @@
         returning,
         skip_gain,
         step_weight,
+        wait,
     )
 
 
@@ -1026,6 +1055,37 @@
     )(place, gate, first, second, *held, *untouched)
 
 
+def early_kernel(place_ref, own_ref, near_ref, far_ref, last_ref, out_ref, gate_ref):
+    rows = own_ref.shape[0]
+    for flip, ref in enumerate((own_ref, far_ref, near_ref, last_ref)):
+        place = place_ref[0] ^ flip
+        at = pl.ds(pl.multiple_of((place & 1) * rows, rows), rows)
+
+        @pl.when(place < 2)
+        def _():
+            out_ref[at, :] = ref[...].astype(f32)
+
+        @pl.when(place >= 2)
+        def _():
+            gate_ref[at, :] = ref[...]
+
+
+def early_joined(place, own, near, far, last):
+    rows, width = own.shape
+    return pl.pallas_call(
+        early_kernel,
+        in_specs=[pl.BlockSpec(memory_space=pltpu.SMEM)]
+        + [pl.BlockSpec(memory_space=pltpu.VMEM)] * 4,
+        out_shape=[
+            jax.ShapeDtypeStruct((2 * rows, width), f32),
+            jax.ShapeDtypeStruct((2 * rows, width), bf16),
+        ],
+        compiler_params=pltpu.CompilerParams(vmem_limit_bytes=vmem_bytes),
+        cost_estimate=tiny_cost,
+        name="early_joined",
+    )(place, own, near, far, last)
+
+
 def through(decay, total):
     return jnp.exp(decay * total)
 
@@ -1150,113 +1210,126 @@
         passed,
         entering,
         skip_gain[None],
-        returning,
-    )
-    products = (
-        lax.dot_general(gated, cot_whole, contract_first, preferred_element_type=f32).astype(bf16),
-        lax.dot_general(normed, gate_grad, contract_first, preferred_element_type=f32).astype(bf16),
-    )
-    out_sum, gate_sum = lax.psum(products, "wide")
+    )
     wide_place = lax.axis_index("wide").astype(jnp.int32)
     four_place = (wide_place & 3)[None]
+    first_bits, *more_bits = group_bits(2)
+    low_bit, high_bit = first_bits
+    whole = whole_low.astype(f32)
 
     def narrow_halves(array):
         low, high = array[:, :features], array[:, features:]
         return jnp.where(right_half, high, low), jnp.where(right_half, low, high)
 
-    def after_forward(products):
-        whole = whole_low.astype(f32)
-        normed_four = quarter_of_four(normed)
-        out_part = jnp.dot(gated, out_weight, preferred_element_type=f32)
-        out_mine, out_other = narrow_halves(out_part)
-        out_theirs = swapped(out_other, "narrow", 1)
-        act_grad, select_grad, scan_small = scan_backward(
-            selected,
-            other_selected,
-            step_pre,
-            step,
-            act,
-            projected,
-            gated_grad,
-            masks,
-            decay_log,
-            entry,
-            passed,
-            returning,
-            skip_gain[None],
-            step_weight,
-        )
-        layer_out = (tokens.astype(f32) + (out_mine + out_theirs)).astype(bf16)
-        inner_main, before, last, conv_small = convolve_grad(
-            select_grad,
-            swapped(select_grad, "narrow", 1),
-            select_weight,
-            act_grad,
-            convolved,
-            act,
-            projected,
-            conv_weight,
-            masks,
-            [out_theirs, *normed_four],
-        )
-        inner_grad = patched(segment_ids, inner_main, last, passed_along(before, "wide", -1))
-        near = swapped(inner_grad, "wide", 2)
-        far = swapped(inner_grad, "wide", 1)
-        keep, *sends = small_quarters(four_place, scan_small, conv_small)
-        smalls = [keep] + [swapped(sends[n - 1], "wide", n) for n in (1, 2, 3)]
-        normed_part = jnp.einsum(
-            "cte,dce->td", jnp.stack([inner_grad, gate_grad]), in_weight, preferred_element_type=f32
-        )
-        gain_part = jnp.sum(normed_part * whole * inverse, axis=0, keepdims=True)
-        row_part = jnp.sum(normed_part * norm_gain * whole, axis=1)[None]
-        normed_mine, normed_other = narrow_halves(normed_part)
-        row_theirs = swapped(row_part, "narrow", 1)
-        normed_theirs = swapped(normed_other, "narrow", 1)
-        near = after(near, *smalls[1:])
-        keep, *sends = inner_quarter(
-            (wide_place >> 2 & 3)[None],
-            inner_grad,
-            near,
-            far,
-            swapped(near, "wide", 1),
-            normed_four,
-            smalls,
-            [row_theirs],
-        )
-        row_sum = (row_part + row_theirs).reshape(rows, 1)
-        gain_mine = jnp.where(right_half, norm_gain[features:], norm_gain[:features])
-        whole_grad = inverse * (gain_mine * (normed_mine + normed_theirs)) - tokens.astype(f32) * (
-            inverse * inverse * inverse
-        ) * (row_sum / (2 * features))
-        tokens_grad = (whole_grad + cotangent.astype(f32)).astype(bf16)
-        first_bits, *more_bits = group_bits(2)
-        gain_sum = gain_part + swapped(gain_part, "narrow", 1)
-        for bit in (bit for bits in more_bits for bit in bits):
-            gain_sum = gain_sum + swapped(gain_sum, "wide", bit)
-        held = keep
-        for n, flip in enumerate(flips(first_bits)[1:]):
-            held = held + swapped(sends[n], "wide", flip).astype(f32)
-        for bits in more_bits:
-            held = scattered(held, bits)
-        held = held.astype(bf16)
-        for bits in reversed(more_bits):
-            held = gathered(held, bits)
-        spare = jnp.broadcast_to(gain_sum, (block_rows - used_rows, gain_sum.shape[1]))
-        held = jnp.concatenate([held[: held.shape[0] - spare.shape[0]], spare.astype(bf16)])
-        held = gathered(held, first_bits)
-        return held, layer_out, tokens_grad
-
-    kinds = jax.eval_shape(after_forward, products)
-    held, layer_out, tokens_grad = lax.cond(
-        segment_ids[0] >= 0,
-        after_forward,
-        lambda pair: jax.tree.map(lambda kind: jnp.zeros(kind.shape, kind.dtype), kinds),
-        products,
-    )
-
-    out_weight_grad = out_sum.astype(f32)
+    def times(left, right):
+        return lax.dot_general(left, right, contract_first, preferred_element_type=f32)
+
+    gated_mine, gated_other = halves_of(gated, 1)
+    normed_mine, normed_other = halves_of(normed, 1)
+    early = jnp.concatenate([times(gated_other, cot_whole), times(normed_other, gate_grad)])
+    arrived = swapped(early.astype(bf16), "wide", 1)
+    early = jnp.concatenate([times(gated_mine, cot_whole), times(normed_mine, gate_grad)])
+    normed_four = quarter_of_four(normed)
+    early, send = folded(early, after(arrived, returning, *normed_four), 2)
+    arrived = swapped(send, "wide", 2)
+    out_part = jnp.dot(gated, out_weight, preferred_element_type=f32)
+    out_mine, out_other = narrow_halves(out_part)
+    out_theirs = swapped(out_other, "narrow", 1)
+    act_grad, select_grad, scan_small = scan_backward(
+        selected,
+        other_selected,
+        step_pre,
+        step,
+        act,
+        projected,
+        gated_grad,
+        masks,
+        decay_log,
+        entry,
+        passed,
+        returning,
+        skip_gain[None],
+        step_weight,
+        send,
+    )
+    layer_out = (tokens.astype(f32) + (out_mine + out_theirs)).astype(bf16)
+    other_select_grad = swapped(select_grad, "narrow", 1)
+    early, send = folded(early, after(arrived, select_grad), low_bit)
+    arrived = swapped(send, "wide", low_bit)
+    inner_main, before, last, conv_small = convolve_grad(
+        select_grad,
+        other_select_grad,
+        select_weight,
+        act_grad,
+        convolved,
+        act,
+        projected,
+        conv_weight,
+        masks,
+        [out_theirs, send],
+    )
+    inner_grad = patched(segment_ids, inner_main, last, passed_along(before, "wide", -1))
+    near = swapped(inner_grad, "wide", 2)
+    far = swapped(inner_grad, "wide", 1)
+    keep, *sends = small_quarters(four_place, scan_small, conv_small)
+    smalls = [keep] + [swapped(sends[n - 1], "wide", n) for n in (1, 2, 3)]
+    early, send = folded(early, after(arrived, inner_grad, *sends), high_bit)
+    arrived = swapped(send, "wide", high_bit)
+    normed_part = jnp.einsum(
+        "cte,dce->td", jnp.stack([inner_grad, gate_grad]), in_weight, preferred_element_type=f32
+    )
+    gain_part = jnp.sum(normed_part * whole * inverse, axis=0, keepdims=True)
+    row_part = jnp.sum(normed_part * norm_gain * whole, axis=1)[None]
+    gain_sum = gain_part + swapped(gain_part, "narrow", 1)
+    for bit in (bit for bits in more_bits for bit in bits):
+        gain_sum = gain_sum + swapped(gain_sum, "wide", bit)
+    normed_mine, normed_other = narrow_halves(normed_part)
+    row_theirs = swapped(row_part, "narrow", 1)
+    normed_theirs = swapped(normed_other, "narrow", 1)
+    near = after(near, send, gain_part, *smalls[1:])
+    last = swapped(near, "wide", 1)
+    early = early + after(arrived, near).astype(f32)
+    for bits in more_bits:
+        early = scattered(early, bits)
+    early = early.astype(bf16)
+    keep, *sends = inner_quarter(
+        (wide_place >> 2 & 3)[None],
+        inner_grad,
+        near,
+        far,
+        last,
+        normed_four,
+        smalls,
+        [row_theirs, early],
+    )
+    for bits in reversed(more_bits):
+        early = gathered(early, bits)
+    early = unfolded(early, after(swapped(early, "wide", high_bit), keep), high_bit)
+    row_sum = (row_part + row_theirs).reshape(rows, 1)
+    gain_mine = jnp.where(right_half, norm_gain[features:], norm_gain[:features])
+    whole_grad = inverse * (gain_mine * (normed_mine + normed_theirs)) - tokens.astype(f32) * (
+        inverse * inverse * inverse
+    ) * (row_sum / (2 * features))
+    tokens_grad = (whole_grad + cotangent.astype(f32)).astype(bf16)
+    arrived = [swapped(sends[n - 1], "wide", flips(first_bits)[n]) for n in (1, 2, 3)]
+    arrived[0] = after(arrived[0], early)
+    held = keep + sum(a.astype(f32) for a in arrived)
+    for bits in more_bits:
+        held = scattered(held, bits)
+    held = held.astype(bf16)
+    for bits in reversed(more_bits):
+        held = gathered(held, bits)
+    spare = jnp.broadcast_to(gain_sum, (block_rows - used_rows, gain_sum.shape[1]))
+    held = jnp.concatenate([held[: held.shape[0] - spare.shape[0]], spare.astype(bf16)])
+    early = unfolded(early, after(swapped(early, "wide", low_bit), held), low_bit)
+    early_near = swapped(early, "wide", 2)
+    early_far = swapped(early, "wide", 1)
+    held = gathered(held, first_bits, early)
     core = swapped(held, "wide", 1)
-    (begun,) = joined(four_place, 0, gate_sum, held, core, (), (out_weight_grad,))
+    out_weight_grad, gate_sum = early_joined(
+        four_place, early, early_near, early_far, swapped(early_near, "wide", 1)
+    )
+    (begun,) = joined(four_place, 0, gate_sum, held, core, (), ())
     near = after(swapped(held, "wide", 2), begun)
     far = swapped(near, "wide", 1)
     conv_at = rank + count + 2

time: 259 us -> 265 us (1.023)
  other arithmetic: 10.2 us -> 26.5 us
  waiting for transfers between devices: 83.6 us -> 67.7 us
  between operations: 14.9 us -> 1.31 us
  Pallas kernels: 76.1 us -> 84.4 us
  starting transfers between devices: 42.6 us -> 48.8 us
  matrix products: 15.7 us -> 19.2 us
  local copies, waits for them, and re-layouts: 12.7 us -> 15.9 us
    ppermute x28 -> x37, waiting for transfers between devices: 76.5 us -> 65.1 us  [swapped(): return lax.ppermute(array, axis, [(i, i ^ bit) for i in range(peers)])]
    add x0 -> x2, other arithmetic: none -> 8.8 us  [rows(): lax.dynamic_slice_in_dim(keep, start, half, 0)]
    unnamed x42 -> x88, local copies, waits for them, and re-layouts: 5.24 us -> 13.3 us
    ppermute x28 -> x37, starting transfers between devices: 30 us -> 35.7 us  [swapped(): return lax.ppermute(array, axis, [(i, i ^ bit) for i in range(peers)])]
    pallas_call x0 -> x1, Pallas kernels: none -> 5.3 us  [early_joined(): pl.pallas_call(early_kernel, in_specs=[pl.BlockSpec(memory_space=pltpu.SM...]
    cond x38 -> x0, local copies, waits for them, and re-layouts: 4.47 us -> none
    ppermute x4, waiting for transfers between devices: 7.08 us -> 2.62 us  [passed_along(): return lax.ppermute(array, axis, pairs)]
    pallas_call x5, Pallas kernels: 50.3 us -> 53.6 us  [call(): pl.pallas_call(kernel, grid=(width // scan_width,), in_specs=in_specs, ou...]
  transfers between devices with their start and end apart: 34 -> 42, of which waited for: 17 -> 19; matrix products, arithmetic and copies ran while one was open for 9% -> 14% of each run, Pallas kernels for 18% -> 20%
where the time goes in v11:
time: 265 us; the launch traced here: 264 us
  Pallas kernels  84.4 us (32%)
  waiting for transfers between devices  67.7 us (26%)
  starting transfers between devices  48.8 us (18%)
  other arithmetic  26.5 us (10%)
  matrix products  19.2 us (7%)
  local copies, waits for them, and re-layouts  15.9 us (6%)
    ppermute x37, waiting for transfers between devices, swapped(): return lax.ppermute(array, axis, [(i, i ^ bit) for i in range(peers)])  65.1 us
    pallas_call x5, Pallas kernels, call(): pl.pallas_call(kernel, grid=(width // scan_width,), in_specs=in_specs, ou...  53.6 us
    ppermute x37, starting transfers between devices, swapped(): return lax.ppermute(array, axis, [(i, i ^ bit) for i in range(peers)])  35.7 us
    unnamed x88, local copies, waits for them, and re-layouts  13.3 us
    ppermute x4, starting transfers between devices, passed_along(): return lax.ppermute(array, axis, pairs)  11.7 us
    pallas_call x2, Pallas kernels, joined(): pl.pallas_call(functools.partial(join_kernel, small_rows=small_rows), gri...  10.8 us
    add x2, other arithmetic, rows(): lax.dynamic_slice_in_dim(keep, start, half, 0)  8.8 us
    dot_general x4, matrix products, times(): lax.dot_general(left, right, contract_first, preferred_element_type=f32)  6.64 us
  transfers between devices with their start and end apart: 42, of which 19 were waited for; matrix products, arithmetic and copies ran while one was open for 14% of the time, Pallas kernels for 20%

profile of v11, /device:TPU:0, one launch (start us, length us, event | category | flops | bytes accessed | tf_op | source)
XLA Modules:
  0.0 263.7 jit_solution(9795683881323705196)
XLA Ops:
  0.7 3.0 %collective-permute-start = (bf16[256,512]{1,0:T(8,128)(2,1)}, bf16[256,512]{1,0:T(8,128)(2,1)S(1)}, u32[]{:S(2)}, u32[]{:S(2)}) collective-permute-start(bf16[256,512]{1,0:T(8,128)(2,1)} %own_ref.1), channel_id=1, source_target_pairs={{0,1},{1,0},{2,3},{3,2},{4,5},{5,4},{6,7},{7,6},{8,9},{9,8},{10,11... | collective-permute-start | bytes 786440 | tf_op jit(solution)/shard_map/ppermute | solution.py:33
  3.7 1.4 edge_rows.1
  5.1 1.4 collective-permute-start.2
  6.5 4.0 %collective-permute-start.1 = (bf16[16,512]{1,0:T(8,128)(2,1)}, bf16[16,512]{1,0:T(8,128)(2,1)S(1)}, u32[]{:S(2)}, u32[]{:S(2)}) collective-permute-start(bf16[16,512]{1,0:T(8,128)(2,1)} %edge_rows.1), channel_id=1, source_target_pairs={{0,2},{2,4},{4,6},{6,8},{8,10},{10,12},{12,14},{14,16},{16,18},{18... | collective-permute-start | bytes 49160 | tf_op jit(solution)/shard_map/ppermute | solution.py:28
  10.5 1.5 collective-permute-start.4
  12.8 2.5 normalized.1
  15.3 5.0 %fusion.12.inner_ref.gate_ref = bf16[2,272,1024]{2,1,0:T(8,128)(2,1)} fusion(bf16[1024,2,1024]{2,1,0:T(2,128)(2,1)} %param.15, bf16[272,1024]{1,0:T(8,128)(2,1)} %get-tuple-element.57), kind=kOutput, calls=%fused_computation.17 | convolution fusion | flops 1141407744 | bytes 5865472 | tf_op jit(solution)/shard_map/td,dce->cte/dot_general | solution.py:1178
  20.2 3.5 %convolve.1 = (f32[256,1024]{1,0:T(8,128)}, bf16[256,1024]{1,0:T(8,128)(2,1)}, f32[96,256]{1,0:T(8,128)}) custom-call(bf16[2,272,1024]{2,1,0:T(8,128)(2,1)} %fusion.12.inner_ref.gate_ref, f32[4,1024]{1,0:T(4,128)} %conv_weight_ref.3, f32[1,1024]{1,0:T(1,128)} %bitcast.39, bf16[96,1024]{1,0:T(8,128)(2,1)} %select_ref.3, f32[256,128]{1,0:T(8,128)} %get-tuple-element.58.mask_ref), custom_call_target="tpu_custom_call" | custom-call | flops 1 | bytes 1 | tf_op jit(solution)/shard_map/convolve/pallas_call | solution.py:155
  24.8 1.8 fusion.37.gated_grad_ref
  26.6 2.0 collective-permute-done.3.other_ref
  29.3 10.8 %scan_ends.1 = (f32[256,1024]{1,0:T(8,128)}, f32[256,1024]{1,0:T(8,128)}, f32[40,1024]{1,0:T(8,128)}) custom-call(f32[96,256]{1,0:T(8,128)} %get-tuple-element.59.selected_ref, f32[96,256]{1,0:T(8,128)} %copy-done.21, bf16[64,1024]{1,0:T(8,128)(2,1)} %step_weight_ref.3, f32[1,1024]{1,0:T(1,128)} %bitcast.40, bf16[256,1024]{1,0:T(8,128)(2,1)} %get-tuple-element.60.act_ref, ...), custom_call_target="tpu_custom_call" | custom-call | flops 1 | bytes 1 | tf_op jit(solution)/shard_map/scan_ends/pallas_call | solution.py:155
  40.1 1.6 collective-permute-done.5.other_ref
  42.4 1.9 carry_round.2
  44.3 1.7 collective-permute-start.6
  46.0 4.8 %collective-permute-done.6.other_ref = f32[40,1024]{1,0:T(8,128)S(1)} collective-permute-done((f32[40,1024]{1,0:T(8,128)}, f32[40,1024]{1,0:T(8,128)S(1)}, u32[]{:S(2)}, u32[]{:S(2)}) %collective-permute-start.6) | collective-permute-done | bytes 163872 | tf_op jit(solution)/shard_map/ppermute | solution.py:33
  51.4 1.9 carry_round.3
  53.3 4.6 %collective-permute-start.7 = (f32[16,1024]{1,0:T(8,128)}, f32[16,1024]{1,0:T(8,128)S(1)}, u32[]{:S(2)}, u32[]{:S(2)}) collective-permute-start(f32[16,1024]{1,0:T(8,128)} %get-tuple-element.66), channel_id=1, source_target_pairs={{0,8},{2,10},{4,12},{6,14},{8,16},{10,18},{12,20},{14,22},{16,24},... | collective-permute-start | bytes 196616 | tf_op jit(solution)/shard_map/ppermute | solution.py:28
  57.9 2.2 collective-permute-done.7.entering_ref
  60.7 10.4 %scan_forward.1 = (bf16[256,1024]{1,0:T(8,128)(2,1)}, bf16[256,1024]{1,0:T(8,128)(2,1)}, f32[16,1024]{1,0:T(8,128)}) custom-call(f32[96,256]{1,0:T(8,128)} %get-tuple-element.59.selected_ref, f32[96,256]{1,0:T(8,128)} %copy-done.21, f32[256,1024]{1,0:T(8,128)} %get-tuple-element.61.step_ref, bf16[256,1024]{1,0:T(8,128)(2,1)} %get-tuple-element.60.act_ref, ...), custom_call_target="tpu_custom_call" | custom-call | flops 1 | bytes 1 | tf_op jit(solution)/shard_map/scan_forward/pallas_call | solution.py:155
  71.2 1.5 convolution_convert_fusion.1
  73.1 1.5 pad_maximum_fusion
  74.6 1.9 constant_dynamic-slice_fusion
  77.2 1.4 collective-permute-start.11
  78.6 1.5 collective-permute-start.9
  80.1 2.9 %fusion.33 = f32[512,1024]{1,0:T(8,128)} fusion(bf16[256,1024]{1,0:T(8,128)(2,1)} %get-tuple-element.73, bf16[256,1024]{1,0:T(8,128)(2,1)} %get-tuple-element.72, s32[]{:T(128)S(6)} %mul.105), kind=kOutput, calls=%fused_computation.55 | convolution fusion | flops 268435456 | bytes 2883588 | tf_op jit(solution)/shard_map/dot_general | solution.py:1225
  83.0 1.8 fusion.35
  85.8 6.0 %fusion.5 = (f32[512,1024]{1,0:T(8,128)}, bf16[512,1024]{1,0:T(8,128)(2,1)}) fusion(s32[]{:T(128)S(6)} %mul.112, f32[512,1024]{1,0:T(8,128)} %fusion.35, f32[512,1024]{1,0:T(8,128)} %fusion.33, bf16[1024,1024]{1,0:T(8,128)(2,1)} %after.10, s32[]{:T(128)S(6)} %select_n.137), kind=kLoop, calls=%fused_computation.9 | loop fusion | flops 3670016 | bytes 9437192 | tf_op jit(solution)/shard_map/add | solution.py:111
  92.4 1.7 fusion.48
  95.0 1.5 collective-permute-start.8
  96.4 24.3 %scan_backward.1 = (f32[256,1024]{1,0:T(8,128)}, f32[96,256]{1,0:T(8,128)}, f32[82,1024]{1,0:T(8,128)}) custom-call(f32[96,256]{1,0:T(8,128)} %get-tuple-element.59.selected_ref, f32[96,256]{1,0:T(8,128)} %copy-done.21, f32[256,1024]{1,0:T(8,128)} %get-tuple-element.69.step_pre_ref, f32[256,1024]{1,0:T(8,128)} %get-tuple-element.61.step_ref, ...), custom_call_target="tpu_custom_call" | custom-call | flops 1 | bytes 1 | tf_op jit(solution)/shard_map/scan_backward/pallas_call | solution.py:155
  120.7 1.6 copy-done.3
  122.3 2.8 %convert_add_fusion = (f32[256,1024]{1,0:T(8,128)}, bf16[256,1024]{1,0:T(8,128)(2,1)}) fusion(f32[512,1024]{1,0:T(8,128)S(1)} %copy-done.3, s32[]{:T(128)S(6)} %mul.126, bf16[512,1024]{1,0:T(8,128)(2,1)} %after.11, s32[]{:T(128)S(6)} %select_n.143), kind=kLoop, calls=%fused_computation.28 | loop fusion | flops 1310720 | bytes 4718600 | tf_op jit(solution)/shard_map/add | solution.py:111
  125.1 2.7 %collective-permute-start.19 = (bf16[256,1024]{1,0:T(8,128)(2,1)}, bf16[256,1024]{1,0:T(8,128)(2,1)}, u32[]{:S(2)}, u32[]{:S(2)}) collective-permute-start(bf16[256,1024]{1,0:T(8,128)(2,1)} %get-tuple-element.109.rest_1_), channel_id=1, source_target_pairs={{0,8},{2,10},{4,12},{6,14},{8,0},{10,2},{12,4},{14,6},{16,24},{18,... | collective-permute-start | bytes 1572872 | tf_op jit(solution)/shard_map/ppermute | solution.py:33
  128.3 4.1 %collective-permute-done.14.other_ref = f32[96,256]{1,0:T(8,128)S(1)} collective-permute-done((f32[96,256]{1,0:T(8,128)S(1)}, f32[96,256]{1,0:T(8,128)S(1)}, u32[]{:S(2)}, u32[]{:S(2)}) %collective-permute-start.14) | collective-permute-done | bytes 98336 | tf_op jit(solution)/shard_map/ppermute | solution.py:33
  133.0 4.6 %convolve_grad.1 = (bf16[256,1024]{1,0:T(8,128)(2,1)}, f32[8,1024]{1,0:T(8,128)}, f32[8,1024]{1,0:T(8,128)}, f32[101,1024]{1,0:T(8,128)}) custom-call(f32[96,256]{1,0:T(8,128)} %get-tuple-element.74.refs_1_.select_grad_ref, f32[96,256]{1,0:T(8,128)} %copy-done.35, bf16[96,1024]{1,0:T(8,128)(2,1)} %select_ref.3, f32[256,1024]{1,0:T(8,128)} %get-tuple-element.75.act_grad_ref, ...), custom_call_target="tpu_custom_call" | custom-call | flops 1 | bytes 1 | tf_op jit(solution)/shard_map/convolve_grad/pallas_call | solution.py:155
  137.7 1.6 collective-permute-start.16
  139.5 2.1 small_quarters.1
  142.7 1.4 collective-permute-start.23
  144.8 1.4 patched.1.refs_1_.own_ref
  146.2 1.4 collective-permute-start.21
  147.6 1.7 add_convert_fusion.2.refs_1_
  149.3 3.5 %collective-permute-start.20 = (bf16[128,1024]{1,0:T(8,128)(2,1)}, bf16[128,1024]{1,0:T(8,128)(2,1)S(1)}, u32[]{:S(2)}, u32[]{:S(2)}) collective-permute-start(bf16[128,1024]{1,0:T(8,128)(2,1)} %add_convert_fusion.2.refs_1_), channel_id=1, source_target_pairs={{0,16},{2,18},{4,20},{6,22},{8,24},{10,26},{12,28},{14,30},{16,0},... | collective-permute-start | bytes 786440 | tf_op jit(solution)/shard_map/ppermute | solution.py:33
  152.8 4.0 %fusion.15 = f32[256,1024]{1,0:T(8,128)S(1)} fusion(bf16[1024,2,1024]{2,1,0:T(2,128)(2,1)} %param.15, bf16[1,256,1024]{2,1,0:T(8,128)(2,1)} %bitcast.31, bf16[1,256,1024]{2,1,0:T(8,128)(2,1)S(1)} %bitcast.30), kind=kOutput, calls=%fused_computation.18 | convolution fusion | flops 1074266112 | bytes 6291456 | tf_op jit(solution)/shard_map/cte,dce->td/dot_general | solution.py:1278
  158.0 4.4 %collective-permute-done.21.refs_0_ = bf16[256,1024]{1,0:T(8,128)(2,1)S(1)} collective-permute-done((bf16[256,1024]{1,0:T(8,128)(2,1)}, bf16[256,1024]{1,0:T(8,128)(2,1)S(1)}, u32[]{:S(2)}, u32[]{:S(2)}) %collective-permute-start.21) | collective-permute-done | bytes 524320 | tf_op jit(solution)/shard_map/ppermute | solution.py:33
  163.2 1.8 collective-permute-done.20.refs_0_
  165.7 1.3 add_convert_fusion.1.rest_1_
  167.0 1.7 collective-permute-start.25
  169.3 3.0 %collective-permute-done.18.rest_0_ = f32[1,256]{1,0:T(1,128)S(1)} collective-permute-done((f32[1,256]{1,0:T(1,128)S(1)}, f32[1,256]{1,0:T(1,128)S(1)}, u32[]{:S(2)}, u32[]{:S(2)}) %collective-permute-start.18) | collective-permute-done | bytes 1056 | tf_op jit(solution)/shard_map/ppermute | solution.py:33
  172.8 3.5 %inner_quarter.1 = (f32[80,1024]{1,0:T(8,128)}, bf16[80,1024]{1,0:T(8,128)(2,1)}, bf16[80,1024]{1,0:T(8,128)(2,1)}, bf16[80,1024]{1,0:T(8,128)(2,1)}) custom-call(s32[1]{0:T(128)} %bitcast.16.place_ref, bf16[256,1024]{1,0:T(8,128)(2,1)} %patched.1.refs_1_.own_ref, bf16[256,1024]{1,0:T(8,128)(2,1)} %after.13.refs_1_.near_ref, ...), custom_call_target="tpu_custom_call" | custom-call | flops 1 | bytes 1 | tf_op jit(solution)/shard_map/inner_quarter/pallas_call | solution.py:968
  176.4 5.2 %collective-permute-done.25.refs_0_ = bf16[128,1024]{1,0:T(8,128)(2,1)S(1)} collective-permute-done((bf16[128,1024]{1,0:T(8,128)(2,1)S(1)}, bf16[128,1024]{1,0:T(8,128)(2,1)S(1)}, u32[]{:S(2)}, u32[]{:S(2)}) %collective-permute-start.25) | collective-permute-done | bytes 262176 | tf_op jit(solution)/shard_map/ppermute | solution.py:33
  183.4 3.2 %collective-permute-start.30 = (bf16[80,1024]{1,0:T(8,128)(2,1)}, bf16[80,1024]{1,0:T(8,128)(2,1)S(1)}, u32[]{:S(2)}, u32[]{:S(2)}) collective-permute-start(bf16[80,1024]{1,0:T(8,128)(2,1)} %get-tuple-element.89), channel_id=1, source_target_pairs={{0,16},{2,18},{4,20},{6,22},{8,24},{10,26},{12,28},{14,30},{16,0},... | collective-permute-start | bytes 491528 | tf_op jit(solution)/shard_map/ppermute | solution.py:33
  189.2 3.0 %collective-permute-done.32 = f32[1,1024]{1,0:T(1,128)S(1)} collective-permute-done((f32[1,1024]{1,0:T(1,128)S(1)}, f32[1,1024]{1,0:T(1,128)S(1)}, u32[]{:S(2)}, u32[]{:S(2)}) %collective-permute-start.32) | collective-permute-done | bytes 4128 | tf_op jit(solution)/shard_map/ppermute | solution.py:33
  192.2 2.1 collective-permute-done.29.refs_0_
  195.0 3.9 %collective-permute-done.30 = bf16[80,1024]{1,0:T(8,128)(2,1)S(1)} collective-permute-done((bf16[80,1024]{1,0:T(8,128)(2,1)}, bf16[80,1024]{1,0:T(8,128)(2,1)S(1)}, u32[]{:S(2)}, u32[]{:S(2)}) %collective-permute-start.30) | collective-permute-done | bytes 163872 | tf_op jit(solution)/shard_map/ppermute | solution.py:33
  201.5 6.5 %collective-permute-done.28.refs_0_ = bf16[256,1024]{1,0:T(8,128)(2,1)S(1)} collective-permute-done((bf16[256,1024]{1,0:T(8,128)(2,1)}, bf16[256,1024]{1,0:T(8,128)(2,1)S(1)}, u32[]{:S(2)}, u32[]{:S(2)}) %collective-permute-start.28) | collective-permute-done | bytes 524320 | tf_op jit(solution)/shard_map/ppermute | solution.py:33
  208.8 1.3 broadcast_select_fusion.1
  211.3 2.4 collective-permute-start.36
  214.4 9.7 %collective-permute-done.37 = bf16[80,1024]{1,0:T(8,128)(2,1)S(1)} collective-permute-done((bf16[80,1024]{1,0:T(8,128)(2,1)S(1)}, bf16[80,1024]{1,0:T(8,128)(2,1)S(1)}, u32[]{:S(2)}, u32[]{:S(2)}) %collective-permute-start.37) | collective-permute-done | bytes 163872 | tf_op jit(solution)/shard_map/ppermute | solution.py:33
  225.3 9.3 %collective-permute-done.33.near_ref = bf16[512,1024]{1,0:T(8,128)(2,1)} collective-permute-done((bf16[512,1024]{1,0:T(8,128)(2,1)S(1)}, bf16[512,1024]{1,0:T(8,128)(2,1)}, u32[]{:S(2)}, u32[]{:S(2)}) %collective-permute-start.33) | collective-permute-done | bytes 1048608 | tf_op jit(solution)/shard_map/ppermute | solution.py:33
  240.5 5.3 %early_joined.1 = (f32[1024,1024]{1,0:T(8,128)}, bf16[1024,1024]{1,0:T(8,128)(2,1)}) custom-call(s32[1]{0:T(128)} %bitcast.14.place_ref, bf16[512,1024]{1,0:T(8,128)(2,1)} %copy-done.2, bf16[512,1024]{1,0:T(8,128)(2,1)} %collective-permute-done.33.near_ref, bf16[512,1024]{1,0:T(8,128)(2,1)} %collective-permute-done.34.far_ref, bf16[512,1024]{1,0:T(8,128)(2,1)} %copy-done.16), custom_call_target="tpu_custom_call" | custom-call | flops 1 | bytes 1 | tf_op jit(solution)/shard_map/early_joined/pallas_call | solution.py:1075
  246.6 4.6 %joined.2.refs_1_.rest_4_ = f32[1024,2,1024]{2,1,0:T(2,128)} custom-call(s32[1]{0:T(128)} %bitcast.14.place_ref, bf16[1024,1024]{1,0:T(8,128)(2,1)} %get-tuple-element.91.gate_ref, bf16[320,1024]{1,0:T(8,128)(2,1)} %copy-done.4, bf16[320,1024]{1,0:T(8,128)(2,1)} %copy-done.8), custom_call_target="tpu_custom_call" | custom-call | flops 1 | bytes 1 | tf_op jit(solution)/shard_map/joined/pallas_call | solution.py:1033
  251.2 2.9 %collective-permute-done.39.refs_0_ = bf16[320,1024]{1,0:T(8,128)(2,1)} collective-permute-done((bf16[320,1024]{1,0:T(8,128)(2,1)S(1)}, bf16[320,1024]{1,0:T(8,128)(2,1)}, u32[]{:S(2)}, u32[]{:S(2)}) %collective-permute-start.39) | collective-permute-done | bytes 655392 | tf_op jit(solution)/shard_map/ppermute | solution.py:33
  254.2 2.2 fusion.29
  257.3 6.2 %joined.3 = (f32[1024,2,1024]{2,1,0:T(2,128)}, f32[64,1024]{1,0:T(8,128)}, f32[16,1024]{1,0:T(8,128)}, f32[1,1024]{1,0:T(1,128)}, f32[1,1024]{1,0:T(1,128)}, /*i...) custom-call(s32[1]{0:T(128)} %bitcast.14.place_ref, ...), custom_call_target="tpu_custom_call", output_to_operand_aliasing={{0}: (8, {})} | custom-call | flops 1 | bytes 1 | tf_op jit(solution)/shard_map/joined/pallas_call | solution.py:1033
  (168 shorter events, 34.3 us)
Async XLA Ops:
  0.6 24.1 %copy-start = (bf16[1024,1024]{1,0:T(8,128)(2,1)S(1)}, bf16[1024,1024]{1,0:T(8,128)(2,1)}, u32[]{:S(2)}) copy-start(bf16[1024,1024]{1,0:T(8,128)(2,1)} %param.23) | copy-start | bytes 6291460
  0.7 11.4 %collective-permute-start = (bf16[256,512]{1,0:T(8,128)(2,1)}, bf16[256,512]{1,0:T(8,128)(2,1)S(1)}, u32[]{:S(2)}, u32[]{:S(2)}) collective-permute-start(bf16[256,512]{1,0:T(8,128)(2,1)} %own_ref.1), channel_id=1, source_target_pairs={{0,1},{1,0},{2,3},{3,2},{4,5},{5,4},{6,7},{7,6},{8,9},{9,8},{10,11... | collective-permute-start | bytes 786440 | tf_op jit(solution)/shard_map/ppermute | solution.py:33
  5.1 7.0 %collective-permute-start.2 = (bf16[16,512]{1,0:T(8,128)(2,1)}, bf16[16,512]{1,0:T(8,128)(2,1)S(1)}, u32[]{:S(2)}, u32[]{:S(2)}) collective-permute-start(bf16[16,512]{1,0:T(8,128)(2,1)} %edge_rows.1), channel_id=1, source_target_pairs={{0,3},{1,2},{2,5},{3,4},{4,7},{5,6},{6,9},{7,8},{8,11},{9,10},{10,... | collective-permute-start | bytes 49160 | tf_op jit(solution)/shard_map/ppermute | solution.py:51
  6.5 5.5 %collective-permute-start.1 = (bf16[16,512]{1,0:T(8,128)(2,1)}, bf16[16,512]{1,0:T(8,128)(2,1)S(1)}, u32[]{:S(2)}, u32[]{:S(2)}) collective-permute-start(bf16[16,512]{1,0:T(8,128)(2,1)} %edge_rows.1), channel_id=1, source_target_pairs={{0,2},{2,4},{4,6},{6,8},{8,10},{10,12},{12,14},{14,16},{16,18},{18... | collective-permute-start | bytes 49160 | tf_op jit(solution)/shard_map/ppermute | solution.py:28
  10.5 14.2 %collective-permute-start.4 = (bf16[256,512]{1,0:T(8,128)(2,1)}, bf16[256,512]{1,0:T(8,128)(2,1)S(1)}, u32[]{:S(2)}, u32[]{:S(2)}) collective-permute-start(bf16[256,512]{1,0:T(8,128)(2,1)} %param.25), channel_id=1, source_target_pairs={{0,1},{1,0},{2,3},{3,2},{4,5},{5,4},{6,7},{7,6},{8,9},{9,8},{10,11... | collective-permute-start | bytes 786440 | tf_op jit(solution)/shard_map/ppermute | solution.py:33
  15.3 9.5 %copy-start.17 = (bf16[256,512]{1,0:T(8,128)(2,1)S(1)}, bf16[256,512]{1,0:T(8,128)(2,1)}, u32[]{:S(2)}) copy-start(bf16[256,512]{1,0:T(8,128)(2,1)} %param.25) | copy-start | bytes 786436
  23.7 4.9 %collective-permute-start.3 = (f32[96,256]{1,0:T(8,128)}, f32[96,256]{1,0:T(8,128)S(1)}, u32[]{:S(2)}, u32[]{:S(2)}) collective-permute-start(f32[96,256]{1,0:T(8,128)} %get-tuple-element.59.selected_ref), channel_id=1, source_target_pairs={{0,1},{1,0},{2,3},{3,2},{4,5},{5,4},{6,7},{7,6},{8,9},{9,8},{10,11... | collective-permute-start | bytes 294920 | tf_op jit(solution)/shard_map/ppermute | solution.py:33
  40.0 1.7 collective-permute-start.5
  44.3 6.5 %collective-permute-start.6 = (f32[40,1024]{1,0:T(8,128)}, f32[40,1024]{1,0:T(8,128)S(1)}, u32[]{:S(2)}, u32[]{:S(2)}) collective-permute-start(f32[40,1024]{1,0:T(8,128)} %get-tuple-element.63.own_ref), channel_id=1, source_target_pairs={{0,4},{2,6},{4,0},{6,2},{8,12},{10,14},{12,8},{14,10},{16,20},{18,... | collective-permute-start | bytes 491528 | tf_op jit(solution)/shard_map/ppermute | solution.py:33
  53.3 6.8 %collective-permute-start.7 = (f32[16,1024]{1,0:T(8,128)}, f32[16,1024]{1,0:T(8,128)S(1)}, u32[]{:S(2)}, u32[]{:S(2)}) collective-permute-start(f32[16,1024]{1,0:T(8,128)} %get-tuple-element.66), channel_id=1, source_target_pairs={{0,8},{2,10},{4,12},{6,14},{8,16},{10,18},{12,20},{14,22},{16,24},... | collective-permute-start | bytes 196616 | tf_op jit(solution)/shard_map/ppermute | solution.py:28
  60.7 11.9 %copy-start.14 = (bf16[256,1024]{1,0:T(8,128)(2,1)S(1)}, bf16[256,1024]{1,0:T(8,128)(2,1)}, u32[]{:S(2)}) copy-start(bf16[256,1024]{1,0:T(8,128)(2,1)} %get-tuple-element.72) | copy-start | bytes 1572868
  71.2 1.5 copy-start.15
  74.6 8.4 %copy-start.13 = (bf16[256,1024]{1,0:T(8,128)(2,1)S(1)}, bf16[256,1024]{1,0:T(8,128)(2,1)}, u32[]{:S(2)}) copy-start(bf16[256,1024]{1,0:T(8,128)(2,1)} %get-tuple-element.67) | copy-start | bytes 1572868
  74.6 10.9 %collective-permute-start.10 = (bf16[1024,1024]{1,0:T(8,128)(2,1)}, bf16[1024,1024]{1,0:T(8,128)(2,1)}, u32[]{:S(2)}, u32[]{:S(2)}) collective-permute-start(bf16[1024,1024]{1,0:T(8,128)(2,1)} %pad_maximum_fusion), channel_id=1, source_target_pairs={{0,2},{2,0},{4,6},{6,4},{8,10},{10,8},{12,14},{14,12},{16,18},{18,... | collective-permute-start | bytes 6291464 | tf_op jit(solution)/shard_map/ppermute | solution.py:33
  76.5 8.3 %collective-permute-start.13 = (bf16[256,256]{1,0:T(8,128)(2,1)S(1)}, bf16[256,256]{1,0:T(8,128)(2,1)S(1)}, u32[]{:S(2)}, u32[]{:S(2)}) collective-permute-start(bf16[256,256]{1,0:T(8,128)(2,1)S(1)} %get-tuple-element.116), channel_id=1, source_target_pairs={{0,6},{2,4},{4,2},{6,0},{8,14},{10,12},{12,10},{14,8},{16,22},{18,... | collective-permute-start | bytes 393224 | tf_op jit(solution)/shard_map/ppermute | solution.py:33
  77.1 7.7 %collective-permute-start.12 = (bf16[256,256]{1,0:T(8,128)(2,1)S(1)}, bf16[256,256]{1,0:T(8,128)(2,1)S(1)}, u32[]{:S(2)}, u32[]{:S(2)}) collective-permute-start(bf16[256,256]{1,0:T(8,128)(2,1)S(1)} %get-tuple-element.117), channel_id=1, source_target_pairs={{0,2},{2,0},{4,6},{6,4},{8,10},{10,8},{12,14},{14,12},{16,18},{18,... | collective-permute-start | bytes 393224 | tf_op jit(solution)/shard_map/ppermute | solution.py:33
  77.2 7.9 %collective-permute-start.11 = (bf16[256,256]{1,0:T(8,128)(2,1)S(1)}, bf16[256,256]{1,0:T(8,128)(2,1)S(1)}, u32[]{:S(2)}, u32[]{:S(2)}) collective-permute-start(bf16[256,256]{1,0:T(8,128)(2,1)S(1)} %get-tuple-element.118), channel_id=1, source_target_pairs={{0,4},{2,6},{4,0},{6,2},{8,12},{10,14},{12,8},{14,10},{16,20},{18,... | collective-permute-start | bytes 393224 | tf_op jit(solution)/shard_map/ppermute | solution.py:33
  78.6 6.9 %collective-permute-start.9 = (f32[16,1024]{1,0:T(8,128)}, f32[16,1024]{1,0:T(8,128)}, u32[]{:S(2)}, u32[]{:S(2)}) collective-permute-start(f32[16,1024]{1,0:T(8,128)} %get-tuple-element.71), channel_id=1, source_target_pairs={{8,0},{10,2},{12,4},{14,6},{16,8},{18,10},{20,12},{22,14},{24,16},... | collective-permute-start | bytes 196616 | tf_op jit(solution)/shard_map/ppermute | solution.py:28
  91.8 28.9 %collective-permute-start.15 = (bf16[512,1024]{1,0:T(8,128)(2,1)}, bf16[512,1024]{1,0:T(8,128)(2,1)}, u32[]{:S(2)}, u32[]{:S(2)}) collective-permute-start(bf16[512,1024]{1,0:T(8,128)(2,1)} %get-tuple-element.107.wait_ref), channel_id=1, source_target_pairs={{0,4},{2,6},{4,0},{6,2},{8,12},{10,14},{12,8},{14,10},{16,20},{18,... | collective-permute-start | bytes 3145736 | tf_op jit(solution)/shard_map/ppermute | solution.py:33
  95.0 33.4 %collective-permute-start.8 = (f32[256,512]{1,0:T(8,128)}, f32[256,512]{1,0:T(8,128)}, u32[]{:S(2)}, u32[]{:S(2)}) collective-permute-start(f32[256,512]{1,0:T(8,128)} %slice_select_fusion.1), channel_id=1, source_target_pairs={{0,1},{1,0},{2,3},{3,2},{4,5},{5,4},{6,7},{7,6},{8,9},{9,8},{10,11... | collective-permute-start | bytes 1572872 | tf_op jit(solution)/shard_map/ppermute | solution.py:33
  120.7 1.6 copy-start.3
  122.3 5.5 %copy-start.29 = (f32[96,256]{1,0:T(8,128)S(1)}, f32[96,256]{1,0:T(8,128)}, u32[]{:S(2)}) copy-start(f32[96,256]{1,0:T(8,128)} %get-tuple-element.74.refs_1_.select_grad_ref) | copy-start | bytes 294916
  125.1 22.5 %collective-permute-start.19 = (bf16[256,1024]{1,0:T(8,128)(2,1)}, bf16[256,1024]{1,0:T(8,128)(2,1)}, u32[]{:S(2)}, u32[]{:S(2)}) collective-permute-start(bf16[256,1024]{1,0:T(8,128)(2,1)} %get-tuple-element.109.rest_1_), channel_id=1, source_target_pairs={{0,8},{2,10},{4,12},{6,14},{8,0},{10,2},{12,4},{14,6},{16,24},{18,... | collective-permute-start | bytes 1572872 | tf_op jit(solution)/shard_map/ppermute | solution.py:33
  127.8 4.6 %collective-permute-start.14 = (f32[96,256]{1,0:T(8,128)S(1)}, f32[96,256]{1,0:T(8,128)S(1)}, u32[]{:S(2)}, u32[]{:S(2)}) collective-permute-start(f32[96,256]{1,0:T(8,128)S(1)} %copy-done.29), channel_id=1, source_target_pairs={{0,1},{1,0},{2,3},{3,2},{4,5},{5,4},{6,7},{7,6},{8,9},{9,8},{10,11... | collective-permute-start | bytes 294920 | tf_op jit(solution)/shard_map/ppermute | solution.py:33
  133.0 6.3 %copy-start.34 = (f32[256,1]{1,0:T(8,128)S(1)}, f32[256,1]{1,0:T(8,128)}, u32[]{:S(2)}) copy-start(f32[256,1]{1,0:T(8,128)} %get-tuple-element.68) | copy-start | bytes 3076
  137.7 9.9 %copy-start.7 = (f32[256,1024]{1,0:T(8,128)S(1)}, f32[256,1024]{1,0:T(8,128)}, u32[]{:S(2)}) copy-start(f32[256,1024]{1,0:T(8,128)} %get-tuple-element.108) | copy-start | bytes 3145732
  137.7 6.5 %collective-permute-start.16 = (f32[8,1024]{1,0:T(8,128)}, f32[8,1024]{1,0:T(8,128)S(1)}, u32[]{:S(2)}, u32[]{:S(2)}) collective-permute-start(f32[8,1024]{1,0:T(8,128)} %get-tuple-element.79), channel_id=1, source_target_pairs={{2,0},{4,2},{6,4},{8,6},{10,8},{12,10},{14,12},{16,14},{18,16},{20... | collective-permute-start | bytes 98312 | tf_op jit(solution)/shard_map/ppermute | solution.py:28
  141.6 16.2 %collective-permute-start.22 = (bf16[64,1024]{1,0:T(8,128)(2,1)}, bf16[64,1024]{1,0:T(8,128)(2,1)S(1)}, u32[]{:S(2)}, u32[]{:S(2)}) collective-permute-start(bf16[64,1024]{1,0:T(8,128)(2,1)} %get-tuple-element.83.refs_2_), channel_id=1, source_target_pairs={{0,2},{2,0},{4,6},{6,4},{8,10},{10,8},{12,14},{14,12},{16,18},{18,... | collective-permute-start | bytes 393224 | tf_op jit(solution)/shard_map/ppermute | solution.py:33
  142.7 15.3 %collective-permute-start.23 = (bf16[64,1024]{1,0:T(8,128)(2,1)}, bf16[64,1024]{1,0:T(8,128)(2,1)}, u32[]{:S(2)}, u32[]{:S(2)}) collective-permute-start(bf16[64,1024]{1,0:T(8,128)(2,1)} %get-tuple-element.84.refs_3_), channel_id=1, source_target_pairs={{0,4},{2,6},{4,0},{6,2},{8,12},{10,14},{12,8},{14,10},{16,20},{18,... | collective-permute-start | bytes 393224 | tf_op jit(solution)/shard_map/ppermute | solution.py:33
  144.2 13.9 %collective-permute-start.24 = (bf16[64,1024]{1,0:T(8,128)(2,1)}, bf16[64,1024]{1,0:T(8,128)(2,1)}, u32[]{:S(2)}, u32[]{:S(2)}) collective-permute-start(bf16[64,1024]{1,0:T(8,128)(2,1)} %get-tuple-element.85.refs_4_), channel_id=1, source_target_pairs={{0,6},{2,4},{4,2},{6,0},{8,14},{10,12},{12,10},{14,8},{16,22},{18,... | collective-permute-start | bytes 393224 | tf_op jit(solution)/shard_map/ppermute | solution.py:33
  146.2 6.5 %copy-start.5 = (bf16[256,1024]{1,0:T(8,128)(2,1)S(1)}, bf16[256,1024]{1,0:T(8,128)(2,1)}, u32[]{:S(2)}) copy-start(bf16[256,1024]{1,0:T(8,128)(2,1)} %patched.1.refs_1_.own_ref) | copy-start | bytes 1572868
  146.2 16.2 %collective-permute-start.21 = (bf16[256,1024]{1,0:T(8,128)(2,1)}, bf16[256,1024]{1,0:T(8,128)(2,1)S(1)}, u32[]{:S(2)}, u32[]{:S(2)}) collective-permute-start(bf16[256,1024]{1,0:T(8,128)(2,1)} %patched.1.refs_1_.own_ref), channel_id=1, source_target_pairs={{0,4},{2,6},{4,0},{6,2},{8,12},{10,14},{12,8},{14,10},{16,20},{18,... | collective-permute-start | bytes 1572872 | tf_op jit(solution)/shard_map/ppermute | solution.py:33
  149.3 15.7 %collective-permute-start.20 = (bf16[128,1024]{1,0:T(8,128)(2,1)}, bf16[128,1024]{1,0:T(8,128)(2,1)S(1)}, u32[]{:S(2)}, u32[]{:S(2)}) collective-permute-start(bf16[128,1024]{1,0:T(8,128)(2,1)} %add_convert_fusion.2.refs_1_), channel_id=1, source_target_pairs={{0,16},{2,18},{4,20},{6,22},{8,24},{10,26},{12,28},{14,30},{16,0},... | collective-permute-start | bytes 786440 | tf_op jit(solution)/shard_map/ppermute | solution.py:33
  152.8 4.0 %copy-start.27 = (bf16[256,1024]{1,0:T(8,128)(2,1)S(1)}, bf16[256,1024]{1,0:T(8,128)(2,1)}, u32[]{:S(2)}) copy-start(bf16[256,1024]{1,0:T(8,128)(2,1)} %get-tuple-element.80) | copy-start | bytes 1572868
  152.8 4.0 %copy-start.38 = (f32[1024]{0:T(1024)S(1)}, f32[1024]{0:T(1024)}, u32[]{:S(2)}) copy-start(f32[1024]{0:T(1024)} %param.14) | copy-start | bytes 12292
  157.8 4.6 %copy-start.28 = (bf16[64,1024]{1,0:T(8,128)(2,1)}, bf16[64,1024]{1,0:T(8,128)(2,1)S(1)}, u32[]{:S(2)}) copy-start(bf16[64,1024]{1,0:T(8,128)(2,1)S(1)} %collective-permute-done.22.refs_3_.first_ref) | copy-start | bytes 393220
  157.8 14.5 %collective-permute-start.26 = (bf16[256,1024]{1,0:T(8,128)(2,1)S(1)}, bf16[256,1024]{1,0:T(8,128)(2,1)}, u32[]{:S(2)}, u32[]{:S(2)}) collective-permute-start(bf16[256,1024]{1,0:T(8,128)(2,1)S(1)} %copy-done.5), channel_id=1, source_target_pairs={{0,2},{2,0},{4,6},{6,4},{8,10},{10,8},{12,14},{14,12},{16,18},{18,... | collective-permute-start | bytes 1572872 | tf_op jit(solution)/shard_map/ppermute | solution.py:33
  163.2 9.1 %collective-permute-start.27 = (bf16[256,1024]{1,0:T(8,128)(2,1)}, bf16[256,1024]{1,0:T(8,128)(2,1)}, u32[]{:S(2)}, u32[]{:S(2)}) collective-permute-start(bf16[256,1024]{1,0:T(8,128)(2,1)} %after.13.refs_1_.near_ref), channel_id=1, source_target_pairs={{0,2},{2,0},{4,6},{6,4},{8,10},{10,8},{12,14},{14,12},{16,18},{18,... | collective-permute-start | bytes 1572872 | tf_op jit(solution)/shard_map/ppermute | solution.py:33
  167.0 5.3 %copy-start.11 = (bf16[128,1024]{1,0:T(8,128)(2,1)}, bf16[128,1024]{1,0:T(8,128)(2,1)S(1)}, u32[]{:S(2)}) copy-start(bf16[128,1024]{1,0:T(8,128)(2,1)S(1)} %add_convert_fusion.1.rest_1_) | copy-start | bytes 786436
  167.0 14.5 %collective-permute-start.25 = (bf16[128,1024]{1,0:T(8,128)(2,1)S(1)}, bf16[128,1024]{1,0:T(8,128)(2,1)S(1)}, u32[]{:S(2)}, u32[]{:S(2)}) collective-permute-start(bf16[128,1024]{1,0:T(8,128)(2,1)S(1)} %add_convert_fusion.1.rest_1_), channel_id=1, source_target_pairs={{0,16},{2,18},{4,20},{6,22},{8,24},{10,26},{12,28},{14,30},{16,0},... | collective-permute-start | bytes 786440 | tf_op jit(solution)/shard_map/ppermute | solution.py:33
  168.7 3.6 %collective-permute-start.18 = (f32[1,256]{1,0:T(1,128)S(1)}, f32[1,256]{1,0:T(1,128)S(1)}, u32[]{:S(2)}, u32[]{:S(2)}) collective-permute-start(f32[1,256]{1,0:T(1,128)S(1)} %bitcast.41), channel_id=1, source_target_pairs={{0,1},{1,0},{2,3},{3,2},{4,5},{5,4},{6,7},{7,6},{8,9},{9,8},{10,11... | collective-permute-start | bytes 3080 | tf_op jit(solution)/shard_map/ppermute | solution.py:33
  176.4 12.2 %copy-start.37 = (f32[1024]{0:T(1024)S(1)}, f32[1024]{0:T(1024)}, u32[]{:S(2)}) copy-start(f32[1024]{0:T(1024)} %get-tuple-element.102) | copy-start | bytes 12292
  183.3 11.0 %collective-permute-start.29 = (bf16[80,1024]{1,0:T(8,128)(2,1)}, bf16[80,1024]{1,0:T(8,128)(2,1)S(1)}, u32[]{:S(2)}, u32[]{:S(2)}) collective-permute-start(bf16[80,1024]{1,0:T(8,128)(2,1)} %get-tuple-element.88), channel_id=1, source_target_pairs={{0,8},{2,10},{4,12},{6,14},{8,0},{10,2},{12,4},{14,6},{16,24},{18,... | collective-permute-start | bytes 491528 | tf_op jit(solution)/shard_map/ppermute | solution.py:33
  183.4 15.5 %collective-permute-start.30 = (bf16[80,1024]{1,0:T(8,128)(2,1)}, bf16[80,1024]{1,0:T(8,128)(2,1)S(1)}, u32[]{:S(2)}, u32[]{:S(2)}) collective-permute-start(bf16[80,1024]{1,0:T(8,128)(2,1)} %get-tuple-element.89), channel_id=1, source_target_pairs={{0,16},{2,18},{4,20},{6,22},{8,24},{10,26},{12,28},{14,30},{16,0},... | collective-permute-start | bytes 491528 | tf_op jit(solution)/shard_map/ppermute | solution.py:33
  186.6 13.0 %collective-permute-start.31 = (bf16[80,1024]{1,0:T(8,128)(2,1)}, bf16[80,1024]{1,0:T(8,128)(2,1)}, u32[]{:S(2)}, u32[]{:S(2)}) collective-permute-start(bf16[80,1024]{1,0:T(8,128)(2,1)} %get-tuple-element.90), channel_id=1, source_target_pairs={{0,24},{2,26},{4,28},{6,30},{8,16},{10,18},{12,20},{14,22},{16,8},... | collective-permute-start | bytes 491528 | tf_op jit(solution)/shard_map/ppermute | solution.py:33
  188.6 19.4 %collective-permute-start.28 = (bf16[256,1024]{1,0:T(8,128)(2,1)}, bf16[256,1024]{1,0:T(8,128)(2,1)S(1)}, u32[]{:S(2)}, u32[]{:S(2)}) collective-permute-start(bf16[256,1024]{1,0:T(8,128)(2,1)} %pad_maximum_fusion.4.refs_1_), channel_id=1, source_target_pairs={{0,8},{2,10},{4,12},{6,14},{8,0},{10,2},{12,4},{14,6},{16,24},{18,... | collective-permute-start | bytes 1572872 | tf_op jit(solution)/shard_map/ppermute | solution.py:33
  188.6 3.6 %collective-permute-start.32 = (f32[1,1024]{1,0:T(1,128)S(1)}, f32[1,1024]{1,0:T(1,128)S(1)}, u32[]{:S(2)}, u32[]{:S(2)}) collective-permute-start(f32[1,1024]{1,0:T(1,128)S(1)} %bitcast.33), channel_id=1, source_target_pairs={{0,1},{1,0},{2,3},{3,2},{4,5},{5,4},{6,7},{7,6},{8,9},{9,8},{10,11... | collective-permute-start | bytes 12296 | tf_op jit(solution)/shard_map/ppermute | solution.py:33
  208.8 2.2 copy-start.22
  210.2 15.1 %copy-start.2 = (bf16[512,1024]{1,0:T(8,128)(2,1)}, bf16[512,1024]{1,0:T(8,128)(2,1)S(1)}, u32[]{:S(2)}) copy-start(bf16[512,1024]{1,0:T(8,128)(2,1)S(1)} %pad_maximum_fusion.1.own_ref.refs_1_) | copy-start | bytes 3145732
  210.2 24.4 %collective-permute-start.33 = (bf16[512,1024]{1,0:T(8,128)(2,1)S(1)}, bf16[512,1024]{1,0:T(8,128)(2,1)}, u32[]{:S(2)}, u32[]{:S(2)}) collective-permute-start(bf16[512,1024]{1,0:T(8,128)(2,1)S(1)} %pad_maximum_fusion.1.own_ref.refs_1_), channel_id=1, source_target_pairs={{0,4},{2,6},{4,0},{6,2},{8,12},{10,14},{12,8},{14,10},{16,20},{18,... | collective-permute-start | bytes 3145736 | tf_op jit(solution)/shard_map/ppermute | solution.py:33
  210.9 13.2 %collective-permute-start.37 = (bf16[80,1024]{1,0:T(8,128)(2,1)S(1)}, bf16[80,1024]{1,0:T(8,128)(2,1)S(1)}, u32[]{:S(2)}, u32[]{:S(2)}) collective-permute-start(bf16[80,1024]{1,0:T(8,128)(2,1)S(1)} %copy-done.22), channel_id=1, source_target_pairs={{0,16},{2,18},{4,20},{6,22},{8,24},{10,26},{12,28},{14,30},{16,0},... | collective-permute-start | bytes 491528 | tf_op jit(solution)/shard_map/ppermute | solution.py:33
  211.3 12.8 %collective-permute-start.36 = (bf16[80,1024]{1,0:T(8,128)(2,1)S(1)}, bf16[80,1024]{1,0:T(8,128)(2,1)S(1)}, u32[]{:S(2)}, u32[]{:S(2)}) collective-permute-start(bf16[80,1024]{1,0:T(8,128)(2,1)S(1)} %copy-done.22), channel_id=1, source_target_pairs={{0,24},{2,26},{4,28},{6,30},{8,16},{10,18},{12,20},{14,22},{16,8},... | collective-permute-start | bytes 491528 | tf_op jit(solution)/shard_map/ppermute | solution.py:33
  213.7 11.7 %collective-permute-start.38 = (bf16[80,1024]{1,0:T(8,128)(2,1)S(1)}, bf16[80,1024]{1,0:T(8,128)(2,1)}, u32[]{:S(2)}, u32[]{:S(2)}) collective-permute-start(bf16[80,1024]{1,0:T(8,128)(2,1)S(1)} %copy-done.22), channel_id=1, source_target_pairs={{0,8},{2,10},{4,12},{6,14},{8,0},{10,2},{12,4},{14,6},{16,24},{18,... | collective-permute-start | bytes 491528 | tf_op jit(solution)/shard_map/ppermute | solution.py:33
  224.8 14.7 %collective-permute-start.34 = (bf16[512,1024]{1,0:T(8,128)(2,1)S(1)}, bf16[512,1024]{1,0:T(8,128)(2,1)}, u32[]{:S(2)}, u32[]{:S(2)}) collective-permute-start(bf16[512,1024]{1,0:T(8,128)(2,1)S(1)} %pad_maximum_fusion.1.own_ref.refs_1_), channel_id=1, source_target_pairs={{0,2},{2,0},{4,6},{6,4},{8,10},{10,8},{12,14},{14,12},{16,18},{18,... | collective-permute-start | bytes 3145736 | tf_op jit(solution)/shard_map/ppermute | solution.py:33
  234.6 4.9 %collective-permute-start.35 = (bf16[512,1024]{1,0:T(8,128)(2,1)}, bf16[512,1024]{1,0:T(8,128)(2,1)S(1)}, u32[]{:S(2)}, u32[]{:S(2)}) collective-permute-start(bf16[512,1024]{1,0:T(8,128)(2,1)} %collective-permute-done.33.near_ref), channel_id=1, source_target_pairs={{0,2},{2,0},{4,6},{6,4},{8,10},{10,8},{12,14},{14,12},{16,18},{18,... | collective-permute-start | bytes 3145736 | tf_op jit(solution)/shard_map/ppermute | solution.py:33
  236.8 9.0 %copy-start.4 = (bf16[320,1024]{1,0:T(8,128)(2,1)}, bf16[320,1024]{1,0:T(8,128)(2,1)S(1)}, u32[]{:S(2)}) copy-start(bf16[320,1024]{1,0:T(8,128)(2,1)S(1)} %pad_maximum_fusion.2.first_ref.rest_0_) | copy-start | bytes 1966084
  236.8 9.0 %collective-permute-start.40 = (bf16[320,1024]{1,0:T(8,128)(2,1)S(1)}, bf16[320,1024]{1,0:T(8,128)(2,1)S(1)}, u32[]{:S(2)}, u32[]{:S(2)}) collective-permute-start(bf16[320,1024]{1,0:T(8,128)(2,1)S(1)} %pad_maximum_fusion.2.first_ref.rest_0_), channel_id=1, source_target_pairs={{0,2},{2,0},{4,6},{6,4},{8,10},{10,8},{12,14},{14,12},{16,18},{18,... | collective-permute-start | bytes 1966088 | tf_op jit(solution)/shard_map/ppermute | solution.py:33
  237.3 16.8 %collective-permute-start.39 = (bf16[320,1024]{1,0:T(8,128)(2,1)S(1)}, bf16[320,1024]{1,0:T(8,128)(2,1)}, u32[]{:S(2)}, u32[]{:S(2)}) collective-permute-start(bf16[320,1024]{1,0:T(8,128)(2,1)S(1)} %pad_maximum_fusion.2.first_ref.rest_0_), channel_id=1, source_target_pairs={{0,4},{2,6},{4,0},{6,2},{8,12},{10,14},{12,8},{14,10},{16,20},{18,... | collective-permute-start | bytes 1966088 | tf_op jit(solution)/shard_map/ppermute | solution.py:33
  238.9 15.3 %collective-permute-start.17 = (f32[256,512]{1,0:T(8,128)}, f32[256,512]{1,0:T(8,128)}, u32[]{:S(2)}, u32[]{:S(2)}) collective-permute-start(f32[256,512]{1,0:T(8,128)} %slice_select_fusion), channel_id=1, source_target_pairs={{0,1},{1,0},{2,3},{3,2},{4,5},{5,4},{6,7},{7,6},{8,9},{9,8},{10,11... | collective-permute-start | bytes 1572872 | tf_op jit(solution)/shard_map/ppermute | solution.py:33
  251.2 2.9 %copy-start.43 = (f32[1,256]{1,0:T(1,128)S(1)}, f32[1,256]{1,0:T(1,128)}, u32[]{:S(2)}) copy-start(f32[1,256]{1,0:T(1,128)} %copy-done.42) | copy-start | bytes 3076
  251.2 3.0 %copy-start.10 = (bf16[256,512]{1,0:T(8,128)(2,1)S(1)}, bf16[256,512]{1,0:T(8,128)(2,1)}, u32[]{:S(2)}) copy-start(bf16[256,512]{1,0:T(8,128)(2,1)} %own_ref.1) | copy-start | bytes 786436
  251.2 3.0 %copy-start.18 = (bf16[256,512]{1,0:T(8,128)(2,1)S(1)}, bf16[256,512]{1,0:T(8,128)(2,1)}, u32[]{:S(2)}) copy-start(bf16[256,512]{1,0:T(8,128)(2,1)} %param.25) | copy-start | bytes 786436
  254.2 2.3 collective-permute-start.41
  257.3 6.2 %copy-start.1 = (bf16[1024,1024]{1,0:T(8,128)(2,1)S(1)}, bf16[1024,1024]{1,0:T(8,128)(2,1)}, u32[]{:S(2)}) copy-start(bf16[1024,1024]{1,0:T(8,128)(2,1)} %param.23) | copy-start | bytes 6291460
  (22 other events, 15.5 us)

commit v12 on v11

--- a/solution.py
+++ b/solution.py
@@ -94,30 +94,22 @@
     return blocks[0]
 
 
-def halves_of(array, axis):
-    upper = is_upper(1).astype(jnp.int32)
-    half = array.shape[axis] // 2
-    return (
-        lax.dynamic_slice_in_dim(array, upper * half, half, axis),
-        lax.dynamic_slice_in_dim(array, (1 - upper) * half, half, axis),
-    )
-
-
-def folded(keep, arrived, bit):
-    half = keep.shape[0] // 2
-    upper = is_upper(bit).astype(jnp.int32)
-
-    def rows(start):
-        return lax.dynamic_slice_in_dim(keep, start, half, 0) + lax.dynamic_slice_in_dim(
-            arrived, start, half, 0
-        ).astype(f32)
-
-    return rows(upper * half), rows((1 - upper) * half).astype(bf16)
-
-
-def unfolded(held, arrived, bit):
-    upper = is_upper(bit)
-    return jnp.concatenate([jnp.where(upper, arrived, held), jnp.where(upper, held, arrived)])
+def early_bits():
+    bits, bit = [], 2
+    while bit < lax.axis_size("wide"):
+        bits.append(bit)
+        bit *= 2
+    return list(zip(bits, bits[1:] + bits[:1]))
+
+
+def early_upper(bits):
+    place = lax.axis_index("wide")
+    return jnp.where(place & 1 == 0, place & bits[0] != 0, place & bits[1] != 0).astype(jnp.int32)[None]
+
+
+def early_swapped(array, bits):
+    peers = lax.axis_size("wide")
+    return lax.ppermute(array, "wide", [(i, i ^ bits[i % 2]) for i in range(peers)])
 
 
 def quarter_of_four(array):
@@ -486,7 +478,8 @@
     returning_ref,
     skip_ref,
     step_weight_ref,
-    wait_ref,
+    first_wait,
+    second_wait,
     act_grad_ref,
     select_grad_ref,
     small_ref,
@@ -601,7 +594,7 @@
     returning,
     skip_gain,
     step_weight,
-    wait,
+    waits,
 ):
     rows, width = step.shape
     count = decay_log.shape[0]
@@ -628,8 +621,8 @@
             column_spec(count),
             column_spec(1),
             column_spec(rank),
-            pl.BlockSpec(memory_space=pl.ANY),
-        ],
+        ]
+        + [pl.BlockSpec(memory_space=pl.ANY)] * 2,
         [column_spec(rows), whole_spec(columns, rows), column_spec(small)],
         [
             jax.ShapeDtypeStruct((rows, width), f32),
@@ -660,7 +653,7 @@
         returning,
         skip_gain,
         step_weight,
-        wait,
+        *waits,
     )
 
 
@@ -825,7 +818,7 @@
     )(array, *waits)
 
 
-def patch_kernel(ids_ref, rows_ref, last_ref, next_ref, out_ref):
+def patch_kernel(ids_ref, rows_ref, last_ref, next_ref, *rest):
     count = ids_ref.shape[0]
     place = lax.broadcasted_iota(jnp.int32, (8, 1), 0)
     same = jnp.zeros((8, 1), f32)
@@ -834,23 +827,24 @@
         same = same + jnp.where(place == 7 - lag, here, 0.0)
     total = last_ref[...] + next_ref[...] * same
     rows = rows_ref[...].astype(f32)
-    out_ref[...] = jnp.concatenate([rows[: halo - 8], total]).astype(bf16)
-
-
-def patched(ids, grads, last, following):
+    rest[-1][...] = jnp.concatenate([rows[: halo - 8], total]).astype(bf16)
+
+
+def patched(ids, grads, last, following, *waits):
     rows, width = grads.shape
     block = pl.BlockSpec((halo, width), lambda j: (rows // halo - 1, 0))
     edge = pl.BlockSpec((8, width), lambda j: (0, 0))
     return pl.pallas_call(
         patch_kernel,
         grid=(1,),
-        in_specs=[pl.BlockSpec(memory_space=pltpu.SMEM), block, edge, edge],
+        in_specs=[pl.BlockSpec(memory_space=pltpu.SMEM), block, edge, edge]
+        + [pl.BlockSpec(memory_space=pl.ANY)] * len(waits),
         out_specs=block,
         out_shape=jax.ShapeDtypeStruct((rows, width), bf16),
         input_output_aliases={1: 0},
         cost_estimate=tiny_cost,
         name="patched",
-    )(ids, grads, last, following)
+    )(ids, grads, last, following, *waits)
 
 
 def edge_kernel(ids_ref, tokens_ref, out_ref):
@@ -884,7 +878,7 @@
 block_rows, used_rows = 16, 12
 
 
-def small_kernel(place_ref, scan_ref, conv_ref, keep_ref, *rest):
+def small_kernel(place_ref, scan_ref, conv_ref, wait_ref, keep_ref, *rest):
     *sends_refs, rows, blocks = rest
     rows[...] = jnp.zeros(rows.shape, f32)
     rows[: scan_ref.shape[0], :] = scan_ref[...]
@@ -904,12 +898,13 @@
             sends_refs[n - 1][...] = block.astype(bf16)
 
 
-def small_quarters(place, scan_small, conv_small):
+def small_quarters(place, scan_small, conv_small, wait):
     width = scan_small.shape[1]
     return pl.pallas_call(
         small_kernel,
         in_specs=[pl.BlockSpec(memory_space=pltpu.SMEM)]
-        + [pl.BlockSpec(memory_space=pltpu.VMEM)] * 2,
+        + [pl.BlockSpec(memory_space=pltpu.VMEM)] * 2
+        + [pl.BlockSpec(memory_space=pl.ANY)],
         out_shape=[jax.ShapeDtypeStruct((4 * block_rows, width), f32)]
         + [jax.ShapeDtypeStruct((4 * block_rows, width), bf16)] * 3,
         scratch_shapes=[
@@ -918,7 +913,7 @@
         ],
         cost_estimate=tiny_cost,
         name="small_quarters",
-    )(place, scan_small, conv_small)
+    )(place, scan_small, conv_small, wait)
 
 
 def quarter_kernel(
@@ -979,12 +974,13 @@
     )(place, own, near, far, last, *normed, *smalls, *waits)
 
 
-def join_kernel(place_ref, gate_ref, first_ref, second_ref, *rest, small_rows):
+def join_kernel(place_ref, own_gate, other_gate, first_ref, second_ref, *rest, small_rows):
     at_end = 2 + len(small_rows) if small_rows else 0
     out_ref = rest[-1 - at_end]
     step = pl.program_id(0)
     rows = out_ref.shape[0] // 2
-    out_ref[:, 1, :] = gate_ref[...].astype(f32)
+    second_core = place_ref[0] & 1 == 1
+    out_ref[:, 1, :] = jnp.where(second_core, own_gate[...], other_gate[...]).astype(f32)
 
     def put(ref):
         for n in range(2):
@@ -1019,8 +1015,8 @@
         )
 
 
-def joined(place, flip, gate, first, second, before, waits, held=(), small_rows=(), small_counts=()):
-    depth, width = gate.shape
+def joined(place, flip, gates, first, second, before, waits, held=(), small_rows=(), small_counts=()):
+    depth, width = gates[0].shape
     quarter = depth // 4
     block = quarter // 2
     piece = first.shape[0] // 2
@@ -1036,6 +1032,7 @@
             num_scalar_prefetch=1,
             grid=(4,),
             in_specs=[
+                pl.BlockSpec((block, width), lambda j, place: (target(j, place), 0)),
                 pl.BlockSpec((block, width), lambda j, place: (target(j, place), 0)),
                 pl.BlockSpec((piece, width), lambda j, place: (jnp.minimum(j, 1), 0)),
                 pl.BlockSpec((piece, width), lambda j, place: (jnp.maximum(j - 2, 0), 0)),
@@ -1048,42 +1045,130 @@
         ),
         out_shape=[jax.ShapeDtypeStruct((depth, 2, width), f32)]
         + [jax.ShapeDtypeStruct((rows, width), f32) for rows in small_counts],
-        input_output_aliases={4 + len(held) + k: k for k in range(len(before))},
+        input_output_aliases={5 + len(held) + k: k for k in range(len(before))},
         compiler_params=pltpu.CompilerParams(vmem_limit_bytes=vmem_bytes),
         cost_estimate=tiny_cost,
         name="joined",
-    )(place, gate, first, second, *held, *untouched)
-
-
-def early_kernel(place_ref, own_ref, near_ref, far_ref, last_ref, out_ref, gate_ref):
-    rows = own_ref.shape[0]
-    for flip, ref in enumerate((own_ref, far_ref, near_ref, last_ref)):
-        place = place_ref[0] ^ flip
-        at = pl.ds(pl.multiple_of((place & 1) * rows, rows), rows)
-
-        @pl.when(place < 2)
-        def _():
-            out_ref[at, :] = ref[...].astype(f32)
-
-        @pl.when(place >= 2)
-        def _():
-            gate_ref[at, :] = ref[...]
-
-
-def early_joined(place, own, near, far, last):
-    rows, width = own.shape
+    )(place, *gates, first, second, *held, *untouched)
+
+
+def small_call(kernel, name, out_shape, scalars, arrays, waits, scratch=()):
     return pl.pallas_call(
-        early_kernel,
-        in_specs=[pl.BlockSpec(memory_space=pltpu.SMEM)]
-        + [pl.BlockSpec(memory_space=pltpu.VMEM)] * 4,
-        out_shape=[
-            jax.ShapeDtypeStruct((2 * rows, width), f32),
-            jax.ShapeDtypeStruct((2 * rows, width), bf16),
-        ],
+        functools.partial(kernel, waits=len(waits)),
+        in_specs=[pl.BlockSpec(memory_space=pltpu.SMEM)] * len(scalars)
+        + [pl.BlockSpec(memory_space=pltpu.VMEM)] * len(arrays)
+        + [pl.BlockSpec(memory_space=pl.ANY)] * len(waits),
+        out_shape=out_shape,
+        scratch_shapes=scratch,
         compiler_params=pltpu.CompilerParams(vmem_limit_bytes=vmem_bytes),
         cost_estimate=tiny_cost,
-        name="early_joined",
-    )(place, own, near, far, last)
+        name=name,
+    )(*scalars, *arrays, *waits)
+
+
+def product_half(left, right, half):
+    size = left.shape[1] // 2
+    return lax.dot_general(
+        left[:, half * size : (half + 1) * size],
+        right[...],
+        contract_first,
+        preferred_element_type=f32,
+    )
+
+
+def early_send_kernel(core_ref, gated_ref, cot_ref, normed_ref, gate_grad_ref, out_ref, *, waits):
+    size = out_ref.shape[0] // 2
+    for core, left, right in ((1, gated_ref, cot_ref), (0, normed_ref, gate_grad_ref)):
+
+        @pl.when(core_ref[0] == core)
+        def _():
+            for half in range(2):
+                rows = slice(half * size, (half + 1) * size)
+                out_ref[rows, :] = product_half(left, right, half).astype(bf16)
+
+
+def early_first_kernel(
+    core_ref,
+    upper_ref,
+    gated_ref,
+    cot_ref,
+    normed_ref,
+    gate_grad_ref,
+    arrived_ref,
+    *rest,
+    waits,
+):
+    keep_ref, send_ref = rest[waits:]
+    size = keep_ref.shape[0]
+    for core, left, right in ((0, gated_ref, cot_ref), (1, normed_ref, gate_grad_ref)):
+        for half in range(2):
+            for mine in range(2):
+
+                @pl.when((core_ref[0] == core) & ((upper_ref[0] == half) == (mine == 1)))
+                def _():
+                    rows = slice(half * size, (half + 1) * size)
+                    total = product_half(left, right, half) + arrived_ref[rows, :].astype(f32)
+                    if mine:
+                        keep_ref[...] = total
+                    else:
+                        send_ref[...] = total.astype(bf16)
+
+
+def fold_kernel(upper_ref, keep_ref, arrived_ref, *rest, waits):
+    out_ref, send_ref = rest[waits:]
+    size = out_ref.shape[0]
+    mine = pl.ds(pl.multiple_of(upper_ref[0] * size, size), size)
+    other = pl.ds(pl.multiple_of((1 - upper_ref[0]) * size, size), size)
+    out_ref[...] = keep_ref[mine, :] + arrived_ref[mine, :].astype(f32)
+    send_ref[...] = (keep_ref[other, :] + arrived_ref[other, :].astype(f32)).astype(bf16)
+
+
+def folded(keep, arrived, bits, *waits):
+    rows, width = keep.shape
+    kinds = [jax.ShapeDtypeStruct((rows // 2, width), kind) for kind in (f32, bf16)]
+    return small_call(fold_kernel, "folded", kinds, [early_upper(bits)], [keep, arrived], waits)
+
+
+def settle_kernel(keep_ref, arrived_ref, *rest, waits):
+    rest[waits][...] = (keep_ref[...] + arrived_ref[...].astype(f32)).astype(bf16)
+
+
+def settled(keep, arrived, *waits):
+    kind = jax.ShapeDtypeStruct(keep.shape, bf16)
+    return small_call(settle_kernel, "settled", kind, [], [keep, arrived], waits)
+
+
+def unfold_kernel(upper_ref, held_ref, arrived_ref, *rest, waits):
+    out_ref = rest[waits]
+    size = held_ref.shape[0]
+    out_ref[pl.ds(pl.multiple_of(upper_ref[0] * size, size), size), :] = held_ref[...]
+    out_ref[pl.ds(pl.multiple_of((1 - upper_ref[0]) * size, size), size), :] = arrived_ref[...]
+
+
+def unfolded(held, arrived, bits, *waits):
+    rows, width = held.shape
+    kind = jax.ShapeDtypeStruct((2 * rows, width), bf16)
+    return small_call(
+        unfold_kernel, "unfolded", kind, [early_upper(bits)], [held, arrived], waits
+    )
+
+
+def widen_kernel(place_ref, own_ref, other_ref, out_ref):
+    out_ref[...] = jnp.where(place_ref[0] & 1 == 1, other_ref[...], own_ref[...]).astype(f32)
+
+
+def widened(place, own, other):
+    rows, width = own.shape
+    block = pl.BlockSpec((rows // 4, width), lambda j: (j, 0))
+    return pl.pallas_call(
+        widen_kernel,
+        grid=(4,),
+        in_specs=[pl.BlockSpec(memory_space=pltpu.SMEM), block, block],
+        out_specs=block,
+        out_shape=jax.ShapeDtypeStruct((rows, width), f32),
+        cost_estimate=tiny_cost,
+        name="widened",
+    )(place, own, other)
 
 
 def through(decay, total):
@@ -1214,26 +1299,31 @@
     wide_place = lax.axis_index("wide").astype(jnp.int32)
     four_place = (wide_place & 3)[None]
     first_bits, *more_bits = group_bits(2)
-    low_bit, high_bit = first_bits
     whole = whole_low.astype(f32)
 
     def narrow_halves(array):
         low, high = array[:, :features], array[:, features:]
         return jnp.where(right_half, high, low), jnp.where(right_half, low, high)
 
-    def times(left, right):
-        return lax.dot_general(left, right, contract_first, preferred_element_type=f32)
-
-    gated_mine, gated_other = halves_of(gated, 1)
-    normed_mine, normed_other = halves_of(normed, 1)
-    early = jnp.concatenate([times(gated_other, cot_whole), times(normed_other, gate_grad)])
-    arrived = swapped(early.astype(bf16), "wide", 1)
-    early = jnp.concatenate([times(gated_mine, cot_whole), times(normed_mine, gate_grad)])
-    normed_four = quarter_of_four(normed)
-    early, send = folded(early, after(arrived, returning, *normed_four), 2)
-    arrived = swapped(send, "wide", 2)
+    steps = early_bits()
+    core = (wide_place & 1)[None]
+    factors = [gated, cot_whole, normed, gate_grad]
+    size, depth = out_weight.shape[0], cot_whole.shape[1]
+    send = small_call(
+        early_send_kernel, "early_send", jax.ShapeDtypeStruct((size, depth), bf16), [core], factors, []
+    )
+    arrived = swapped(send, "wide", 1)
     out_part = jnp.dot(gated, out_weight, preferred_element_type=f32)
     out_mine, out_other = narrow_halves(out_part)
+    early, send = small_call(
+        early_first_kernel,
+        "early_first",
+        [jax.ShapeDtypeStruct((size // 2, depth), kind) for kind in (f32, bf16)],
+        [core, early_upper(steps[0])],
+        [*factors, arrived],
+        [out_other, returning],
+    )
+    arrived = early_swapped(send, steps[0])
     out_theirs = swapped(out_other, "narrow", 1)
     act_grad, select_grad, scan_small = scan_backward(
         selected,
@@ -1250,15 +1340,13 @@
         returning,
         skip_gain[None],
         step_weight,
-        send,
+        [send, out_other],
     )
     layer_out = (tokens.astype(f32) + (out_mine + out_theirs)).astype(bf16)
-    other_select_grad = swapped(select_grad, "narrow", 1)
-    early, send = folded(early, after(arrived, select_grad), low_bit)
-    arrived = swapped(send, "wide", low_bit)
+    normed_four = quarter_of_four(after(normed, select_grad))
     inner_main, before, last, conv_small = convolve_grad(
         select_grad,
-        other_select_grad,
+        swapped(select_grad, "narrow", 1),
         select_weight,
         act_grad,
         convolved,
@@ -1266,15 +1354,16 @@
         projected,
         conv_weight,
         masks,
-        [out_theirs, send],
-    )
-    inner_grad = patched(segment_ids, inner_main, last, passed_along(before, "wide", -1))
+        [out_theirs],
+    )
+    following = passed_along(before, "wide", -1)
+    early, send = folded(early, arrived, steps[1], conv_small)
+    arrived = early_swapped(send, steps[1])
+    inner_grad = patched(segment_ids, inner_main, last, following, send, *normed_four)
     near = swapped(inner_grad, "wide", 2)
     far = swapped(inner_grad, "wide", 1)
-    keep, *sends = small_quarters(four_place, scan_small, conv_small)
+    keep, *sends = small_quarters(four_place, scan_small, conv_small, inner_grad)
     smalls = [keep] + [swapped(sends[n - 1], "wide", n) for n in (1, 2, 3)]
-    early, send = folded(early, after(arrived, inner_grad, *sends), high_bit)
-    arrived = swapped(send, "wide", high_bit)
     normed_part = jnp.einsum(
         "cte,dce->td", jnp.stack([inner_grad, gate_grad]), in_weight, preferred_element_type=f32
     )
@@ -1283,15 +1372,16 @@
     gain_sum = gain_part + swapped(gain_part, "narrow", 1)
     for bit in (bit for bits in more_bits for bit in bits):
         gain_sum = gain_sum + swapped(gain_sum, "wide", bit)
+    for bits in steps[2:]:
+        early, send = folded(early, arrived, bits, gain_part, *sends)
+        arrived = early_swapped(send, bits)
     normed_mine, normed_other = narrow_halves(normed_part)
     row_theirs = swapped(row_part, "narrow", 1)
     normed_theirs = swapped(normed_other, "narrow", 1)
-    near = after(near, send, gain_part, *smalls[1:])
+    near = after(near, send, gain_sum, row_theirs, *smalls[1:])
     last = swapped(near, "wide", 1)
-    early = early + after(arrived, near).astype(f32)
-    for bits in more_bits:
-        early = scattered(early, bits)
-    early = early.astype(bf16)
+    early = settled(early, arrived, near)
+    back = early_swapped(early, steps[-1])
     keep, *sends = inner_quarter(
         (wide_place >> 2 & 3)[None],
         inner_grad,
@@ -1300,11 +1390,11 @@
         last,
         normed_four,
         smalls,
-        [row_theirs, early],
-    )
-    for bits in reversed(more_bits):
-        early = gathered(early, bits)
-    early = unfolded(early, after(swapped(early, "wide", high_bit), keep), high_bit)
+        [early],
+    )
+    for bits, following_bits in zip(steps[:1:-1], steps[-2:0:-1]):
+        early = unfolded(early, back, bits, keep)
+        back = early_swapped(early, following_bits)
     row_sum = (row_part + row_theirs).reshape(rows, 1)
     gain_mine = jnp.where(right_half, norm_gain[features:], norm_gain[:features])
     whole_grad = inverse * (gain_mine * (normed_mine + normed_theirs)) - tokens.astype(f32) * (
@@ -1312,7 +1402,7 @@
     ) * (row_sum / (2 * features))
     tokens_grad = (whole_grad + cotangent.astype(f32)).astype(bf16)
     arrived = [swapped(sends[n - 1], "wide", flips(first_bits)[n]) for n in (1, 2, 3)]
-    arrived[0] = after(arrived[0], early)
+    arrived[0] = after(arrived[0], early, normed_theirs)
     held = keep + sum(a.astype(f32) for a in arrived)
     for bits in more_bits:
         held = scattered(held, bits)
@@ -1321,15 +1411,15 @@
         held = gathered(held, bits)
     spare = jnp.broadcast_to(gain_sum, (block_rows - used_rows, gain_sum.shape[1]))
     held = jnp.concatenate([held[: held.shape[0] - spare.shape[0]], spare.astype(bf16)])
-    early = unfolded(early, after(swapped(early, "wide", low_bit), held), low_bit)
-    early_near = swapped(early, "wide", 2)
-    early_far = swapped(early, "wide", 1)
+    early = unfolded(early, back, steps[1], held)
+    back = early_swapped(early, steps[0])
     held = gathered(held, first_bits, early)
     core = swapped(held, "wide", 1)
-    out_weight_grad, gate_sum = early_joined(
-        four_place, early, early_near, early_far, swapped(early_near, "wide", 1)
-    )
-    (begun,) = joined(four_place, 0, gate_sum, held, core, (), ())
+    early = unfolded(early, back, steps[0], core)
+    core_early = swapped(early, "wide", 1)
+    out_weight_grad = widened(four_place, early, core_early)
+    gates = (early, core_early)
+    (begun,) = joined(four_place, 0, gates, held, core, (), (out_weight_grad,))
     near = after(swapped(held, "wide", 2), begun)
     far = swapped(near, "wide", 1)
     conv_at = rank + count + 2
@@ -1346,7 +1436,7 @@
     ) = joined(
         four_place,
         2,
-        gate_sum,
+        gates,
         near,
         far,
         (begun,),

time: 265 us -> 263 us (level)
  Pallas kernels: 84.4 us -> 107 us
  other arithmetic: 26.5 us -> 12 us
  matrix products: 19.2 us -> 12.4 us
  waiting for transfers between devices: 67.7 us -> 62.1 us
    ppermute x37 -> x30, waiting for transfers between devices: 65.1 us -> 28.3 us  [swapped(): return lax.ppermute(array, axis, [(i, i ^ bit) for i in range(peers)])]
    ppermute x0 -> x6, waiting for transfers between devices: none -> 29.5 us  [early_swapped(): lax.ppermute(array, 'wide', [(i, i ^ bits[i % 2]) for i in range(peers)])]
    pallas_call x1 -> x9, Pallas kernels: 5.3 us -> 27.9 us  [the longest x8 23.2 us: small_call(): pl.pallas_call(functools.partial(kernel, waits=len(waits)), in_specs=[pl....]
    add x2 -> x0, other arithmetic: 8.8 us -> none  [rows(): lax.dynamic_slice_in_dim(keep, start, half, 0)]
    dot_general x4 -> x0, matrix products: 6.64 us -> none  [times(): lax.dot_general(left, right, contract_first, preferred_element_type=f32)]
    ppermute x0 -> x6, starting transfers between devices: none -> 5.98 us  [early_swapped(): lax.ppermute(array, 'wide', [(i, i ^ bits[i % 2]) for i in range(peers)])]
    ppermute x37 -> x30, starting transfers between devices: 35.7 us -> 32.1 us  [swapped(): return lax.ppermute(array, axis, [(i, i ^ bit) for i in range(peers)])]
    convert_element_type x2 -> x0, other arithmetic: 2.99 us -> none  [the longest x1 1.71 us: folded(): return (rows(upper * half), rows((1 - upper) * half).astype(bf16))]
  transfers between devices with their start and end apart: 42 -> 41, of which waited for: 19 -> 17; matrix products, arithmetic and copies ran while one was open for 14% -> 10% of each run, Pallas kernels for 20% -> 25%
where the time goes in v12:
time: 263 us; the launch traced here: 262 us
  Pallas kernels  107 us (41%)
  waiting for transfers between devices  62.1 us (24%)
  starting transfers between devices  50.9 us (19%)
  local copies, waits for them, and re-layouts  15.9 us (6%)
  matrix products  12.4 us (5%)
  other arithmetic  12 us (5%)
    pallas_call x5, Pallas kernels, call(): pl.pallas_call(kernel, grid=(width // scan_width,), in_specs=in_specs, ou...  53.6 us
    ppermute x30, starting transfers between devices, swapped(): return lax.ppermute(array, axis, [(i, i ^ bit) for i in range(peers)])  32.1 us
    ppermute x6, waiting for transfers between devices, early_swapped(): lax.ppermute(array, 'wide', [(i, i ^ bits[i % 2]) for i in range(peers)])  29.5 us
    ppermute x30, waiting for transfers between devices, swapped(): return lax.ppermute(array, axis, [(i, i ^ bit) for i in range(peers)])  28.3 us
    pallas_call x8, Pallas kernels, small_call(): pl.pallas_call(functools.partial(kernel, waits=len(waits)), in_specs=[pl....  23.2 us
    unnamed x96, local copies, waits for them, and re-layouts  13.3 us
    ppermute x4, starting transfers between devices, passed_along(): return lax.ppermute(array, axis, pairs)  11.3 us
    pallas_call x2, Pallas kernels, joined(): pl.pallas_call(functools.partial(join_kernel, small_rows=small_rows), gri...  11.2 us
  transfers between devices with their start and end apart: 41, of which 17 were waited for; matrix products, arithmetic and copies ran while one was open for 10% of the time, Pallas kernels for 25%

profile of v12, /device:TPU:0, one launch (start us, length us, event | category | flops | bytes accessed | tf_op | source)
XLA Modules:
  0.0 262.1 jit_solution(2040003020269628149)
XLA Ops:
  0.7 3.0 %collective-permute-start = (bf16[256,512]{1,0:T(8,128)(2,1)}, bf16[256,512]{1,0:T(8,128)(2,1)S(1)}, u32[]{:S(2)}, u32[]{:S(2)}) collective-permute-start(bf16[256,512]{1,0:T(8,128)(2,1)} %own_ref.1), channel_id=1, source_target_pairs={{0,1},{1,0},{2,3},{3,2},{4,5},{5,4},{6,7},{7,6},{8,9},{9,8},{10,11... | collective-permute-start | bytes 786440 | tf_op jit(solution)/shard_map/ppermute | solution.py:33
  3.7 1.4 edge_rows.1
  5.1 1.4 collective-permute-start.2
  6.5 4.0 %collective-permute-start.1 = (bf16[16,512]{1,0:T(8,128)(2,1)}, bf16[16,512]{1,0:T(8,128)(2,1)S(1)}, u32[]{:S(2)}, u32[]{:S(2)}) collective-permute-start(bf16[16,512]{1,0:T(8,128)(2,1)} %edge_rows.1), channel_id=1, source_target_pairs={{0,2},{2,4},{4,6},{6,8},{8,10},{10,12},{12,14},{14,16},{16,18},{18... | collective-permute-start | bytes 49160 | tf_op jit(solution)/shard_map/ppermute | solution.py:28
  10.5 1.5 collective-permute-start.4
  12.8 2.5 normalized.1
  15.3 4.9 %fusion.7.inner_ref.gate_ref = bf16[2,272,1024]{2,1,0:T(8,128)(2,1)} fusion(bf16[1024,2,1024]{2,1,0:T(2,128)(2,1)} %param.15, bf16[272,1024]{1,0:T(8,128)(2,1)} %get-tuple-element.61), kind=kOutput, calls=%fused_computation.5 | convolution fusion | flops 1141407744 | bytes 5865472 | tf_op jit(solution)/shard_map/td,dce->cte/dot_general | solution.py:1263
  20.2 3.5 %convolve.1 = (f32[256,1024]{1,0:T(8,128)}, bf16[256,1024]{1,0:T(8,128)(2,1)}, f32[96,256]{1,0:T(8,128)}) custom-call(bf16[2,272,1024]{2,1,0:T(8,128)(2,1)} %fusion.7.inner_ref.gate_ref, f32[4,1024]{1,0:T(4,128)} %conv_weight_ref.3, f32[1,1024]{1,0:T(1,128)} %bitcast.41, bf16[96,1024]{1,0:T(8,128)(2,1)} %select_ref.3, f32[256,128]{1,0:T(8,128)} %get-tuple-element.62.mask_ref), custom_call_target="tpu_custom_call" | custom-call | flops 1 | bytes 1 | tf_op jit(solution)/shard_map/convolve/pallas_call | solution.py:147
  24.8 1.7 fusion.28.gated_grad_ref
  26.6 2.1 collective-permute-done.3.other_ref
  29.3 10.7 %scan_ends.1 = (f32[256,1024]{1,0:T(8,128)}, f32[256,1024]{1,0:T(8,128)}, f32[40,1024]{1,0:T(8,128)}) custom-call(f32[96,256]{1,0:T(8,128)} %get-tuple-element.63.selected_ref, f32[96,256]{1,0:T(8,128)} %copy-done.19, bf16[64,1024]{1,0:T(8,128)(2,1)} %step_weight_ref.3, f32[1,1024]{1,0:T(1,128)} %bitcast.42, bf16[256,1024]{1,0:T(8,128)(2,1)} %get-tuple-element.64.act_ref, ...), custom_call_target="tpu_custom_call" | custom-call | flops 1 | bytes 1 | tf_op jit(solution)/shard_map/scan_ends/pallas_call | solution.py:147
  40.1 1.6 collective-permute-done.5.other_ref
  42.4 1.9 carry_round.2
  44.3 1.7 collective-permute-start.6
  46.0 4.8 %collective-permute-done.6.other_ref = f32[40,1024]{1,0:T(8,128)S(1)} collective-permute-done((f32[40,1024]{1,0:T(8,128)}, f32[40,1024]{1,0:T(8,128)S(1)}, u32[]{:S(2)}, u32[]{:S(2)}) %collective-permute-start.6) | collective-permute-done | bytes 163872 | tf_op jit(solution)/shard_map/ppermute | solution.py:33
  51.4 1.9 carry_round.3
  53.3 4.6 %collective-permute-start.7 = (f32[16,1024]{1,0:T(8,128)}, f32[16,1024]{1,0:T(8,128)S(1)}, u32[]{:S(2)}, u32[]{:S(2)}) collective-permute-start(f32[16,1024]{1,0:T(8,128)} %get-tuple-element.70), channel_id=1, source_target_pairs={{0,8},{2,10},{4,12},{6,14},{8,16},{10,18},{12,20},{14,22},{16,24},... | collective-permute-start | bytes 196616 | tf_op jit(solution)/shard_map/ppermute | solution.py:28
  58.7 1.3 collective-permute-done.7.entering_ref
  60.7 10.4 %scan_forward.1 = (bf16[256,1024]{1,0:T(8,128)(2,1)}, bf16[256,1024]{1,0:T(8,128)(2,1)}, f32[16,1024]{1,0:T(8,128)}) custom-call(f32[96,256]{1,0:T(8,128)} %get-tuple-element.63.selected_ref, f32[96,256]{1,0:T(8,128)} %copy-done.19, f32[256,1024]{1,0:T(8,128)} %get-tuple-element.65.step_ref, bf16[256,1024]{1,0:T(8,128)(2,1)} %get-tuple-element.64.act_ref, ...), custom_call_target="tpu_custom_call" | custom-call | flops 1 | bytes 1 | tf_op jit(solution)/shard_map/scan_forward/pallas_call | solution.py:147
  71.1 3.6 %early_send.1 = bf16[1024,1024]{1,0:T(8,128)(2,1)} custom-call(s32[1]{0:T(128)} %bitcast.9.core_ref, bf16[256,1024]{1,0:T(8,128)(2,1)} %get-tuple-element.71.gated_ref, bf16[256,1024]{1,0:T(8,128)(2,1)} %pad_maximum_fusion.1.cot_ref, bf16[256,1024]{1,0:T(8,128)(2,1)} %get-tuple-element.76.normed_ref.refs_0_, bf16[256,1024]{1,0:T(8,128)(2,1)} %get-tuple-element.77.gate_grad_ref), custom_call_target="tpu_custom_call" | custom-call | flops 1 | bytes 1 | tf_op jit(solution)/shard_map/early_send/pallas_call | solution.py:1056
  74.8 1.3 collective-permute-start.9
  76.1 1.7 fusion.30
  78.7 3.0 %collective-permute-done.9.rest_1_.returning_ref = f32[16,1024]{1,0:T(8,128)S(1)} collective-permute-done((f32[16,1024]{1,0:T(8,128)S(1)}, f32[16,1024]{1,0:T(8,128)S(1)}, u32[]{:S(2)}, u32[]{:S(2)}) %collective-permute-start.9) | collective-permute-done | bytes 65568 | tf_op jit(solution)/shard_map/ppermute | solution.py:28
  82.3 5.2 %early_first.1 = (f32[512,1024]{1,0:T(8,128)}, bf16[512,1024]{1,0:T(8,128)(2,1)}) custom-call(s32[1]{0:T(128)} %bitcast.9.core_ref, s32[1]{0:T(128)} %bitcast.10.upper_ref, bf16[256,1024]{1,0:T(8,128)(2,1)} %get-tuple-element.71.gated_ref, bf16[256,1024]{1,0:T(8,128)(2,1)} %pad_maximum_fusion.1.cot_ref, ...), custom_call_target="tpu_custom_call" | custom-call | flops 1 | bytes 1 | tf_op jit(solution)/shard_map/early_first/pallas_call | solution.py:1056
  88.1 1.5 collective-permute-start.8
  89.5 24.3 %scan_backward.1 = (f32[256,1024]{1,0:T(8,128)}, f32[96,256]{1,0:T(8,128)}, f32[82,1024]{1,0:T(8,128)}) custom-call(f32[96,256]{1,0:T(8,128)} %get-tuple-element.63.selected_ref, f32[96,256]{1,0:T(8,128)} %copy-done.19, f32[256,1024]{1,0:T(8,128)} %get-tuple-element.73.step_pre_ref, f32[256,1024]{1,0:T(8,128)} %get-tuple-element.65.step_ref, ...), custom_call_target="tpu_custom_call" | custom-call | flops 1 | bytes 1 | tf_op jit(solution)/shard_map/scan_backward/pallas_call | solution.py:147
  114.4 1.9 constant_dynamic-slice_fusion
  116.5 1.4 collective-permute-start.15
  119.2 4.7 %convolve_grad.1 = (bf16[256,1024]{1,0:T(8,128)(2,1)}, f32[8,1024]{1,0:T(8,128)}, f32[8,1024]{1,0:T(8,128)}, f32[101,1024]{1,0:T(8,128)}) custom-call(f32[96,256]{1,0:T(8,128)} %get-tuple-element.79.select_grad_ref.refs_1_, f32[96,256]{1,0:T(8,128)} %collective-permute-done.11.other_ref, bf16[96,1024]{1,0:T(8,128)(2,1)} %select_ref.3, ...), custom_call_target="tpu_custom_call" | custom-call | flops 1 | bytes 1 | tf_op jit(solution)/shard_map/convolve_grad/pallas_call | solution.py:147
  123.8 1.5 collective-permute-start.12
  127.0 3.2 %folded.2 = (f32[256,1024]{1,0:T(8,128)}, bf16[256,1024]{1,0:T(8,128)(2,1)}) custom-call(s32[1]{0:T(128)} %bitcast.11.upper_ref, f32[512,1024]{1,0:T(8,128)} %get-tuple-element.85.keep_ref, bf16[512,1024]{1,0:T(8,128)(2,1)} %copy-done.18, f32[101,1024]{1,0:T(8,128)} %get-tuple-element.86.rest_0_.conv_ref), custom_call_target="tpu_custom_call" | custom-call | flops 1 | bytes 1 | tf_op jit(solution)/shard_map/folded/pallas_call | solution.py:1056
  130.3 2.2 collective-permute-start.19
  133.2 1.4 patched.1.wait_ref.own_ref
  134.6 1.3 collective-permute-start.21
  136.0 4.0 %fusion.10 = f32[256,1024]{1,0:T(8,128)S(1)} fusion(bf16[1024,2,1024]{2,1,0:T(2,128)(2,1)} %param.15, bf16[1,256,1024]{2,1,0:T(8,128)(2,1)S(1)} %bitcast.33, bf16[1,256,1024]{2,1,0:T(8,128)(2,1)} %bitcast.32), kind=kOutput, calls=%fused_computation.6 | convolution fusion | flops 1074266112 | bytes 6291456 | tf_op jit(solution)/shard_map/cte,dce->td/dot_general | solution.py:1367
  140.9 1.5 collective-permute-start.22
  142.3 2.1 small_quarters.1
  146.9 1.3 convert_reduce_fusion
  148.2 2.3 folded.3
  151.2 2.0 collective-permute-start.20
  153.2 2.1 collective-permute-done.25.refs_6_.third_ref
  157.7 1.4 collective-permute-start.17
  159.1 2.4 collective-permute-done.20.arrived_ref
  161.6 1.9 settled.1.rest_0_.held_ref
  164.2 3.5 %inner_quarter.1 = (f32[80,1024]{1,0:T(8,128)}, bf16[80,1024]{1,0:T(8,128)(2,1)}, bf16[80,1024]{1,0:T(8,128)(2,1)}, bf16[80,1024]{1,0:T(8,128)(2,1)}) custom-call(s32[1]{0:T(128)} %bitcast.20.place_ref, bf16[256,1024]{1,0:T(8,128)(2,1)} %patched.1.wait_ref.own_ref, bf16[256,1024]{1,0:T(8,128)(2,1)} %after.6.rest_0_.near_ref, ...), custom_call_target="tpu_custom_call" | custom-call | flops 1 | bytes 1 | tf_op jit(solution)/shard_map/inner_quarter/pallas_call | solution.py:963
  167.8 3.1 %collective-permute-start.30 = (bf16[80,1024]{1,0:T(8,128)(2,1)}, bf16[80,1024]{1,0:T(8,128)(2,1)S(1)}, u32[]{:S(2)}, u32[]{:S(2)}) collective-permute-start(bf16[80,1024]{1,0:T(8,128)(2,1)} %get-tuple-element.98), channel_id=1, source_target_pairs={{0,8},{2,10},{4,12},{6,14},{8,0},{10,2},{12,4},{14,6},{16,24},{18,... | collective-permute-start | bytes 491528 | tf_op jit(solution)/shard_map/ppermute | solution.py:33
  170.9 2.4 collective-permute-start.32
  173.3 14.8 %collective-permute-done.26.arrived_ref = bf16[128,1024]{1,0:T(8,128)(2,1)} collective-permute-done((bf16[128,1024]{1,0:T(8,128)(2,1)}, bf16[128,1024]{1,0:T(8,128)(2,1)}, u32[]{:S(2)}, u32[]{:S(2)}) %collective-permute-start.26) | collective-permute-done | bytes 262176 | tf_op jit(solution)/shard_map/ppermute | solution.py:112
  188.1 1.9 unfolded.3.refs_1_.held_ref
  192.6 5.5 %collective-permute-start.35 = (bf16[80,1024]{1,0:T(8,128)(2,1)S(1)}, bf16[80,1024]{1,0:T(8,128)(2,1)S(1)}, u32[]{:S(2)}, u32[]{:S(2)}) collective-permute-start(bf16[80,1024]{1,0:T(8,128)(2,1)S(1)} %pad_maximum_fusion.4.rest_0_), channel_id=1, source_target_pairs={{0,16},{2,18},{4,20},{6,22},{8,24},{10,26},{12,28},{14,30},{16,0},... | collective-permute-start | bytes 491528 | tf_op jit(solution)/shard_map/ppermute | solution.py:33
  199.1 6.9 %collective-permute-done.35 = bf16[80,1024]{1,0:T(8,128)(2,1)S(1)} collective-permute-done((bf16[80,1024]{1,0:T(8,128)(2,1)S(1)}, bf16[80,1024]{1,0:T(8,128)(2,1)S(1)}, u32[]{:S(2)}, u32[]{:S(2)}) %collective-permute-start.35) | collective-permute-done | bytes 163872 | tf_op jit(solution)/shard_map/ppermute | solution.py:33
  206.0 2.3 collective-permute-done.34
  209.0 3.4 %collective-permute-done.29.arrived_ref = bf16[256,1024]{1,0:T(8,128)(2,1)S(1)} collective-permute-done((bf16[256,1024]{1,0:T(8,128)(2,1)}, bf16[256,1024]{1,0:T(8,128)(2,1)S(1)}, u32[]{:S(2)}, u32[]{:S(2)}) %collective-permute-start.29) | collective-permute-done | bytes 524320 | tf_op jit(solution)/shard_map/ppermute | solution.py:112
  213.2 2.2 unfolded.4.refs_1_.held_ref
  219.3 2.3 collective-permute-done.37.rest_0_.second_ref.rest_1_
  221.6 8.8 %collective-permute-done.33.arrived_ref = bf16[512,1024]{1,0:T(8,128)(2,1)S(1)} collective-permute-done((bf16[512,1024]{1,0:T(8,128)(2,1)}, bf16[512,1024]{1,0:T(8,128)(2,1)S(1)}, u32[]{:S(2)}, u32[]{:S(2)}) %collective-permute-start.33) | collective-permute-done | bytes 1048608 | tf_op jit(solution)/shard_map/ppermute | solution.py:112
  231.4 3.0 %unfolded.5.own_ref.own_gate = bf16[1024,1024]{1,0:T(8,128)(2,1)} custom-call(s32[1]{0:T(128)} %bitcast.10.upper_ref, bf16[512,1024]{1,0:T(8,128)(2,1)} %unfolded.4.refs_1_.held_ref, bf16[512,1024]{1,0:T(8,128)(2,1)} %copy-done.16, bf16[320,1024]{1,0:T(8,128)(2,1)} %copy-done.5), custom_call_target="tpu_custom_call" | custom-call | flops 1 | bytes 1 | tf_op jit(solution)/shard_map/unfolded/pallas_call | solution.py:1056
  235.5 3.3 %collective-permute-done.38.other_ref.other_gate = bf16[1024,1024]{1,0:T(8,128)(2,1)S(1)} collective-permute-done((bf16[1024,1024]{1,0:T(8,128)(2,1)}, bf16[1024,1024]{1,0:T(8,128)(2,1)S(1)}, u32[]{:S(2)}, u32[]{:S(2)}) %collective-permute-start.38) | collective-permute-done | bytes 2097184 | tf_op jit(solution)/shard_map/ppermute | solution.py:33
  238.8 1.3 copy-done.2
  240.1 4.7 %widened.1.rest_0_ = f32[1024,1024]{1,0:T(8,128)} custom-call(s32[1]{0:T(128)} %bitcast.17.place_ref, bf16[1024,1024]{1,0:T(8,128)(2,1)} %unfolded.5.own_ref.own_gate, bf16[1024,1024]{1,0:T(8,128)(2,1)} %copy-done.2), custom_call_target="tpu_custom_call" | custom-call | flops 1 | bytes 1 | tf_op jit(solution)/shard_map/widened/pallas_call | solution.py:1163
  244.8 4.8 %joined.2.refs_1_.rest_4_ = f32[1024,2,1024]{2,1,0:T(2,128)} custom-call(s32[1]{0:T(128)} %bitcast.17.place_ref, bf16[1024,1024]{1,0:T(8,128)(2,1)} %unfolded.5.own_ref.own_gate, bf16[1024,1024]{1,0:T(8,128)(2,1)} %copy-done.2, bf16[320,1024]{1,0:T(8,128)(2,1)} %pad_maximum_fusion.first_ref.rest_0_, bf16[320,1024]{1,0:T(8,128)(2,1)} %copy-done.5, ...), custom_call_target="tpu_custom_call" | custom-call | flops 1 | bytes 1 | tf_op jit(solution)/shard_map/joined/pallas_call | solution.py:1029
  249.6 2.2 collective-permute-done.39.refs_0_
  252.6 2.1 fusion.24
  255.5 6.4 %joined.3 = (f32[1024,2,1024]{2,1,0:T(2,128)}, f32[64,1024]{1,0:T(8,128)}, f32[16,1024]{1,0:T(8,128)}, f32[1,1024]{1,0:T(1,128)}, f32[1,1024]{1,0:T(1,128)}, /*i...) custom-call(s32[1]{0:T(128)} %bitcast.17.place_ref, ...), custom_call_target="tpu_custom_call", output_to_operand_aliasing={{0}: (9, {})} | custom-call | flops 1 | bytes 1 | tf_op jit(solution)/shard_map/joined/pallas_call | solution.py:1029
  (165 shorter events, 31.6 us)
Async XLA Ops:
  0.6 24.2 %copy-start = (bf16[1024,1024]{1,0:T(8,128)(2,1)S(1)}, bf16[1024,1024]{1,0:T(8,128)(2,1)}, u32[]{:S(2)}) copy-start(bf16[1024,1024]{1,0:T(8,128)(2,1)} %param.23) | copy-start | bytes 6291460
  0.7 11.4 %collective-permute-start = (bf16[256,512]{1,0:T(8,128)(2,1)}, bf16[256,512]{1,0:T(8,128)(2,1)S(1)}, u32[]{:S(2)}, u32[]{:S(2)}) collective-permute-start(bf16[256,512]{1,0:T(8,128)(2,1)} %own_ref.1), channel_id=1, source_target_pairs={{0,1},{1,0},{2,3},{3,2},{4,5},{5,4},{6,7},{7,6},{8,9},{9,8},{10,11... | collective-permute-start | bytes 786440 | tf_op jit(solution)/shard_map/ppermute | solution.py:33
  5.1 7.0 %collective-permute-start.2 = (bf16[16,512]{1,0:T(8,128)(2,1)}, bf16[16,512]{1,0:T(8,128)(2,1)S(1)}, u32[]{:S(2)}, u32[]{:S(2)}) collective-permute-start(bf16[16,512]{1,0:T(8,128)(2,1)} %edge_rows.1), channel_id=1, source_target_pairs={{0,3},{1,2},{2,5},{3,4},{4,7},{5,6},{6,9},{7,8},{8,11},{9,10},{10,... | collective-permute-start | bytes 49160 | tf_op jit(solution)/shard_map/ppermute | solution.py:51
  6.5 5.5 %collective-permute-start.1 = (bf16[16,512]{1,0:T(8,128)(2,1)}, bf16[16,512]{1,0:T(8,128)(2,1)S(1)}, u32[]{:S(2)}, u32[]{:S(2)}) collective-permute-start(bf16[16,512]{1,0:T(8,128)(2,1)} %edge_rows.1), channel_id=1, source_target_pairs={{0,2},{2,4},{4,6},{6,8},{8,10},{10,12},{12,14},{14,16},{16,18},{18... | collective-permute-start | bytes 49160 | tf_op jit(solution)/shard_map/ppermute | solution.py:28
  10.5 14.3 %collective-permute-start.4 = (bf16[256,512]{1,0:T(8,128)(2,1)}, bf16[256,512]{1,0:T(8,128)(2,1)S(1)}, u32[]{:S(2)}, u32[]{:S(2)}) collective-permute-start(bf16[256,512]{1,0:T(8,128)(2,1)} %param.25), channel_id=1, source_target_pairs={{0,1},{1,0},{2,3},{3,2},{4,5},{5,4},{6,7},{7,6},{8,9},{9,8},{10,11... | collective-permute-start | bytes 786440 | tf_op jit(solution)/shard_map/ppermute | solution.py:33
  15.3 9.5 %copy-start.17 = (bf16[256,512]{1,0:T(8,128)(2,1)S(1)}, bf16[256,512]{1,0:T(8,128)(2,1)}, u32[]{:S(2)}) copy-start(bf16[256,512]{1,0:T(8,128)(2,1)} %param.25) | copy-start | bytes 786436
  23.8 4.9 %collective-permute-start.3 = (f32[96,256]{1,0:T(8,128)}, f32[96,256]{1,0:T(8,128)S(1)}, u32[]{:S(2)}, u32[]{:S(2)}) collective-permute-start(f32[96,256]{1,0:T(8,128)} %get-tuple-element.63.selected_ref), channel_id=1, source_target_pairs={{0,1},{1,0},{2,3},{3,2},{4,5},{5,4},{6,7},{7,6},{8,9},{9,8},{10,11... | collective-permute-start | bytes 294920 | tf_op jit(solution)/shard_map/ppermute | solution.py:33
  40.0 1.7 collective-permute-start.5
  44.3 6.5 %collective-permute-start.6 = (f32[40,1024]{1,0:T(8,128)}, f32[40,1024]{1,0:T(8,128)S(1)}, u32[]{:S(2)}, u32[]{:S(2)}) collective-permute-start(f32[40,1024]{1,0:T(8,128)} %get-tuple-element.67.own_ref), channel_id=1, source_target_pairs={{0,4},{2,6},{4,0},{6,2},{8,12},{10,14},{12,8},{14,10},{16,20},{18,... | collective-permute-start | bytes 491528 | tf_op jit(solution)/shard_map/ppermute | solution.py:33
  53.3 6.8 %collective-permute-start.7 = (f32[16,1024]{1,0:T(8,128)}, f32[16,1024]{1,0:T(8,128)S(1)}, u32[]{:S(2)}, u32[]{:S(2)}) collective-permute-start(f32[16,1024]{1,0:T(8,128)} %get-tuple-element.70), channel_id=1, source_target_pairs={{0,8},{2,10},{4,12},{6,14},{8,16},{10,18},{12,20},{14,22},{16,24},... | collective-permute-start | bytes 196616 | tf_op jit(solution)/shard_map/ppermute | solution.py:28
  71.1 3.6 %copy-start.47 = (f32[16,1024]{1,0:T(8,128)S(1)}, f32[16,1024]{1,0:T(8,128)}, u32[]{:S(2)}) copy-start(f32[16,1024]{1,0:T(8,128)} %get-tuple-element.75) | copy-start | bytes 196612
  74.8 6.9 %collective-permute-start.10 = (bf16[1024,1024]{1,0:T(8,128)(2,1)}, bf16[1024,1024]{1,0:T(8,128)(2,1)}, u32[]{:S(2)}, u32[]{:S(2)}) collective-permute-start(bf16[1024,1024]{1,0:T(8,128)(2,1)} %early_send.1), channel_id=1, source_target_pairs={{0,2},{2,0},{4,6},{6,4},{8,10},{10,8},{12,14},{14,12},{16,18},{18,... | collective-permute-start | bytes 6291464 | tf_op jit(solution)/shard_map/ppermute | solution.py:33
  74.8 6.9 %collective-permute-start.9 = (f32[16,1024]{1,0:T(8,128)S(1)}, f32[16,1024]{1,0:T(8,128)S(1)}, u32[]{:S(2)}, u32[]{:S(2)}) collective-permute-start(f32[16,1024]{1,0:T(8,128)S(1)} %copy-done.47), channel_id=1, source_target_pairs={{8,0},{10,2},{12,4},{14,6},{16,8},{18,10},{20,12},{22,14},{24,16},... | collective-permute-start | bytes 196616 | tf_op jit(solution)/shard_map/ppermute | solution.py:28
  82.3 5.8 %copy-start.7 = (f32[256,512]{1,0:T(8,128)S(1)}, f32[256,512]{1,0:T(8,128)}, u32[]{:S(2)}) copy-start(f32[256,512]{1,0:T(8,128)} %slice_select_fusion.1.rest_0_.second_wait) | copy-start | bytes 1572868
  87.5 38.6 %collective-permute-start.13 = (bf16[512,1024]{1,0:T(8,128)(2,1)}, bf16[512,1024]{1,0:T(8,128)(2,1)S(1)}, u32[]{:S(2)}, u32[]{:S(2)}) collective-permute-start(bf16[512,1024]{1,0:T(8,128)(2,1)} %get-tuple-element.78.first_wait), channel_id=1, source_target_pairs={{0,4},{2,10},{4,0},{6,14},{8,12},{10,2},{12,8},{14,6},{16,20},{18,... | collective-permute-start | bytes 3145736 | tf_op jit(solution)/shard_map/ppermute | solution.py:112
  88.1 29.8 %collective-permute-start.8 = (f32[256,512]{1,0:T(8,128)S(1)}, f32[256,512]{1,0:T(8,128)S(1)}, u32[]{:S(2)}, u32[]{:S(2)}) collective-permute-start(f32[256,512]{1,0:T(8,128)S(1)} %copy-done.7), channel_id=1, source_target_pairs={{0,1},{1,0},{2,3},{3,2},{4,5},{5,4},{6,7},{7,6},{8,9},{9,8},{10,11... | collective-permute-start | bytes 1572872 | tf_op jit(solution)/shard_map/ppermute | solution.py:33
  113.8 5.3 %collective-permute-start.11 = (f32[96,256]{1,0:T(8,128)}, f32[96,256]{1,0:T(8,128)}, u32[]{:S(2)}, u32[]{:S(2)}) collective-permute-start(f32[96,256]{1,0:T(8,128)} %get-tuple-element.79.select_grad_ref.refs_1_), channel_id=1, source_target_pairs={{0,1},{1,0},{2,3},{3,2},{4,5},{5,4},{6,7},{7,6},{8,9},{9,8},{10,11... | collective-permute-start | bytes 294920 | tf_op jit(solution)/shard_map/ppermute | solution.py:33
  116.3 16.2 %collective-permute-start.16 = (bf16[256,256]{1,0:T(8,128)(2,1)}, bf16[256,256]{1,0:T(8,128)(2,1)S(1)}, u32[]{:S(2)}, u32[]{:S(2)}) collective-permute-start(bf16[256,256]{1,0:T(8,128)(2,1)} %get-tuple-element.118), channel_id=1, source_target_pairs={{0,6},{2,4},{4,2},{6,0},{8,14},{10,12},{12,10},{14,8},{16,22},{18,... | collective-permute-start | bytes 393224 | tf_op jit(solution)/shard_map/ppermute | solution.py:33
  116.5 16.0 %collective-permute-start.15 = (bf16[256,256]{1,0:T(8,128)(2,1)}, bf16[256,256]{1,0:T(8,128)(2,1)}, u32[]{:S(2)}, u32[]{:S(2)}) collective-permute-start(bf16[256,256]{1,0:T(8,128)(2,1)} %get-tuple-element.119), channel_id=1, source_target_pairs={{0,2},{2,0},{4,6},{6,4},{8,10},{10,8},{12,14},{14,12},{16,18},{18,... | collective-permute-start | bytes 393224 | tf_op jit(solution)/shard_map/ppermute | solution.py:33
  117.9 14.7 %collective-permute-start.14 = (bf16[256,256]{1,0:T(8,128)(2,1)}, bf16[256,256]{1,0:T(8,128)(2,1)S(1)}, u32[]{:S(2)}, u32[]{:S(2)}) collective-permute-start(bf16[256,256]{1,0:T(8,128)(2,1)} %get-tuple-element.120), channel_id=1, source_target_pairs={{0,4},{2,6},{4,0},{6,2},{8,12},{10,14},{12,8},{14,10},{16,20},{18,... | collective-permute-start | bytes 393224 | tf_op jit(solution)/shard_map/ppermute | solution.py:33
  119.2 6.2 %copy-start.36 = (f32[256,1]{1,0:T(8,128)S(1)}, f32[256,1]{1,0:T(8,128)}, u32[]{:S(2)}) copy-start(f32[256,1]{1,0:T(8,128)} %get-tuple-element.72) | copy-start | bytes 3076
  123.8 8.7 %collective-permute-start.12 = (f32[8,1024]{1,0:T(8,128)}, f32[8,1024]{1,0:T(8,128)S(1)}, u32[]{:S(2)}, u32[]{:S(2)}) collective-permute-start(f32[8,1024]{1,0:T(8,128)} %get-tuple-element.84), channel_id=1, source_target_pairs={{2,0},{4,2},{6,4},{8,6},{10,8},{12,10},{14,12},{16,14},{18,16},{20... | collective-permute-start | bytes 98312 | tf_op jit(solution)/shard_map/ppermute | solution.py:28
  127.0 8.9 %copy-start.13 = (bf16[256,1024]{1,0:T(8,128)(2,1)S(1)}, bf16[256,1024]{1,0:T(8,128)(2,1)}, u32[]{:S(2)}) copy-start(bf16[256,1024]{1,0:T(8,128)(2,1)} %get-tuple-element.77.gate_grad_ref) | copy-start | bytes 1572868
  130.3 16.1 %collective-permute-start.19 = (bf16[256,1024]{1,0:T(8,128)(2,1)}, bf16[256,1024]{1,0:T(8,128)(2,1)}, u32[]{:S(2)}, u32[]{:S(2)}) collective-permute-start(bf16[256,1024]{1,0:T(8,128)(2,1)} %get-tuple-element.87.rest_0_), channel_id=1, source_target_pairs={{0,8},{2,18},{4,12},{6,22},{8,0},{10,26},{12,4},{14,30},{16,24},{1... | collective-permute-start | bytes 1572872 | tf_op jit(solution)/shard_map/ppermute | solution.py:112
  134.6 20.6 %collective-permute-start.21 = (bf16[256,1024]{1,0:T(8,128)(2,1)}, bf16[256,1024]{1,0:T(8,128)(2,1)S(1)}, u32[]{:S(2)}, u32[]{:S(2)}) collective-permute-start(bf16[256,1024]{1,0:T(8,128)(2,1)} %patched.1.wait_ref.own_ref), channel_id=1, source_target_pairs={{0,4},{2,6},{4,0},{6,2},{8,12},{10,14},{12,8},{14,10},{16,20},{18,... | collective-permute-start | bytes 1572872 | tf_op jit(solution)/shard_map/ppermute | solution.py:33
  136.0 4.0 %copy-start.25 = (bf16[256,1024]{1,0:T(8,128)(2,1)S(1)}, bf16[256,1024]{1,0:T(8,128)(2,1)}, u32[]{:S(2)}) copy-start(bf16[256,1024]{1,0:T(8,128)(2,1)} %get-tuple-element.88) | copy-start | bytes 1572868
  136.0 4.0 %copy-start.39 = (f32[1024]{0:T(1024)S(1)}, f32[1024]{0:T(1024)}, u32[]{:S(2)}) copy-start(f32[1024]{0:T(1024)} %param.14) | copy-start | bytes 12292
  140.0 16.8 %copy-start.3 = (f32[256,1024]{1,0:T(8,128)}, f32[256,1024]{1,0:T(8,128)S(1)}, u32[]{:S(2)}) copy-start(f32[256,1024]{1,0:T(8,128)S(1)} %fusion.10) | copy-start | bytes 3145732
  140.0 10.5 %copy-start.8 = (bf16[256,1024]{1,0:T(8,128)(2,1)S(1)}, bf16[256,1024]{1,0:T(8,128)(2,1)}, u32[]{:S(2)}) copy-start(bf16[256,1024]{1,0:T(8,128)(2,1)} %patched.1.wait_ref.own_ref) | copy-start | bytes 1572868
  140.9 7.4 %copy-start.38 = (f32[1024]{0:T(1024)}, f32[1024]{0:T(1024)S(1)}, u32[]{:S(2)}) copy-start(f32[1024]{0:T(1024)S(1)} %get-tuple-element.110) | copy-start | bytes 12292
  140.9 4.7 %collective-permute-start.22 = (f32[1,1024]{1,0:T(1,128)S(1)}, f32[1,1024]{1,0:T(1,128)S(1)}, u32[]{:S(2)}, u32[]{:S(2)}) collective-permute-start(f32[1,1024]{1,0:T(1,128)S(1)} %bitcast.34), channel_id=1, source_target_pairs={{0,1},{1,0},{2,3},{3,2},{4,5},{5,4},{6,7},{7,6},{8,9},{9,8},{10,11... | collective-permute-start | bytes 12296 | tf_op jit(solution)/shard_map/ppermute | solution.py:33
  144.5 6.7 %collective-permute-start.23 = (bf16[64,1024]{1,0:T(8,128)(2,1)}, bf16[64,1024]{1,0:T(8,128)(2,1)S(1)}, u32[]{:S(2)}, u32[]{:S(2)}) collective-permute-start(bf16[64,1024]{1,0:T(8,128)(2,1)} %get-tuple-element.91.rest_1_), channel_id=1, source_target_pairs={{0,2},{2,0},{4,6},{6,4},{8,10},{10,8},{12,14},{14,12},{16,18},{18,... | collective-permute-start | bytes 393224 | tf_op jit(solution)/shard_map/ppermute | solution.py:33
  144.7 8.5 %collective-permute-start.24 = (bf16[64,1024]{1,0:T(8,128)(2,1)}, bf16[64,1024]{1,0:T(8,128)(2,1)S(1)}, u32[]{:S(2)}, u32[]{:S(2)}) collective-permute-start(bf16[64,1024]{1,0:T(8,128)(2,1)} %get-tuple-element.92.rest_2_), channel_id=1, source_target_pairs={{0,4},{2,6},{4,0},{6,2},{8,12},{10,14},{12,8},{14,10},{16,20},{18,... | collective-permute-start | bytes 393224 | tf_op jit(solution)/shard_map/ppermute | solution.py:33
  145.5 9.7 %collective-permute-start.25 = (bf16[64,1024]{1,0:T(8,128)(2,1)}, bf16[64,1024]{1,0:T(8,128)(2,1)S(1)}, u32[]{:S(2)}, u32[]{:S(2)}) collective-permute-start(bf16[64,1024]{1,0:T(8,128)(2,1)} %get-tuple-element.93.rest_3_), channel_id=1, source_target_pairs={{0,6},{2,4},{4,2},{6,0},{8,14},{10,12},{12,10},{14,8},{16,22},{18,... | collective-permute-start | bytes 393224 | tf_op jit(solution)/shard_map/ppermute | solution.py:33
  146.3 4.2 %collective-permute-start.18 = (f32[1,256]{1,0:T(1,128)}, f32[1,256]{1,0:T(1,128)S(1)}, u32[]{:S(2)}, u32[]{:S(2)}) collective-permute-start(f32[1,256]{1,0:T(1,128)} %bitcast.15), channel_id=1, source_target_pairs={{0,1},{1,0},{2,3},{3,2},{4,5},{5,4},{6,7},{7,6},{8,9},{9,8},{10,11... | collective-permute-start | bytes 3080 | tf_op jit(solution)/shard_map/ppermute | solution.py:33
  150.6 4.7 %copy-start.43 = (f32[1,256]{1,0:T(1,128)}, f32[1,256]{1,0:T(1,128)S(1)}, u32[]{:S(2)}) copy-start(f32[1,256]{1,0:T(1,128)S(1)} %collective-permute-done.18.refs_3_) | copy-start | bytes 3076
  150.6 12.9 %collective-permute-start.27 = (bf16[256,1024]{1,0:T(8,128)(2,1)S(1)}, bf16[256,1024]{1,0:T(8,128)(2,1)}, u32[]{:S(2)}, u32[]{:S(2)}) collective-permute-start(bf16[256,1024]{1,0:T(8,128)(2,1)S(1)} %copy-done.8), channel_id=1, source_target_pairs={{0,2},{2,0},{4,6},{6,4},{8,10},{10,8},{12,14},{14,12},{16,18},{18,... | collective-permute-start | bytes 1572872 | tf_op jit(solution)/shard_map/ppermute | solution.py:33
  151.2 4.8 %copy-start.27 = (bf16[64,1024]{1,0:T(8,128)(2,1)}, bf16[64,1024]{1,0:T(8,128)(2,1)S(1)}, u32[]{:S(2)}) copy-start(bf16[64,1024]{1,0:T(8,128)(2,1)S(1)} %collective-permute-done.23.refs_4_.first_ref) | copy-start | bytes 393220
  151.2 10.4 %collective-permute-start.20 = (bf16[128,1024]{1,0:T(8,128)(2,1)}, bf16[128,1024]{1,0:T(8,128)(2,1)}, u32[]{:S(2)}, u32[]{:S(2)}) collective-permute-start(bf16[128,1024]{1,0:T(8,128)(2,1)} %get-tuple-element.95.refs_1_), channel_id=1, source_target_pairs={{0,16},{2,6},{4,20},{6,2},{8,24},{10,14},{12,28},{14,10},{16,0},{1... | collective-permute-start | bytes 786440 | tf_op jit(solution)/shard_map/ppermute | solution.py:112
  153.2 2.1 copy-start.28
  156.7 6.7 %collective-permute-start.28 = (bf16[256,1024]{1,0:T(8,128)(2,1)}, bf16[256,1024]{1,0:T(8,128)(2,1)S(1)}, u32[]{:S(2)}, u32[]{:S(2)}) collective-permute-start(bf16[256,1024]{1,0:T(8,128)(2,1)} %after.6.rest_0_.near_ref), channel_id=1, source_target_pairs={{0,2},{2,0},{4,6},{6,4},{8,10},{10,8},{12,14},{14,12},{16,18},{18,... | collective-permute-start | bytes 1572872 | tf_op jit(solution)/shard_map/ppermute | solution.py:33
  157.7 32.3 %collective-permute-start.17 = (f32[256,512]{1,0:T(8,128)}, f32[256,512]{1,0:T(8,128)S(1)}, u32[]{:S(2)}, u32[]{:S(2)}) collective-permute-start(f32[256,512]{1,0:T(8,128)} %slice_select_fusion), channel_id=1, source_target_pairs={{0,1},{1,0},{2,3},{3,2},{4,5},{5,4},{6,7},{7,6},{8,9},{9,8},{10,11... | collective-permute-start | bytes 1572872 | tf_op jit(solution)/shard_map/ppermute | solution.py:33
  163.4 24.7 %collective-permute-start.26 = (bf16[128,1024]{1,0:T(8,128)(2,1)}, bf16[128,1024]{1,0:T(8,128)(2,1)}, u32[]{:S(2)}, u32[]{:S(2)}) collective-permute-start(bf16[128,1024]{1,0:T(8,128)(2,1)} %settled.1.rest_0_.held_ref), channel_id=1, source_target_pairs={{0,16},{2,6},{4,20},{6,2},{8,24},{10,14},{12,28},{14,10},{16,0},{1... | collective-permute-start | bytes 786440 | tf_op jit(solution)/shard_map/ppermute | solution.py:112
  167.8 23.8 %copy-start.15 = (f32[80,1024]{1,0:T(8,128)S(1)}, f32[80,1024]{1,0:T(8,128)}, u32[]{:S(2)}) copy-start(f32[80,1024]{1,0:T(8,128)} %get-tuple-element.97.rest_0_) | copy-start | bytes 983044
  167.8 22.2 %collective-permute-start.30 = (bf16[80,1024]{1,0:T(8,128)(2,1)}, bf16[80,1024]{1,0:T(8,128)(2,1)S(1)}, u32[]{:S(2)}, u32[]{:S(2)}) collective-permute-start(bf16[80,1024]{1,0:T(8,128)(2,1)} %get-tuple-element.98), channel_id=1, source_target_pairs={{0,8},{2,10},{4,12},{6,14},{8,0},{10,2},{12,4},{14,6},{16,24},{18,... | collective-permute-start | bytes 491528 | tf_op jit(solution)/shard_map/ppermute | solution.py:33
  170.9 20.7 %collective-permute-start.31 = (bf16[80,1024]{1,0:T(8,128)(2,1)}, bf16[80,1024]{1,0:T(8,128)(2,1)S(1)}, u32[]{:S(2)}, u32[]{:S(2)}) collective-permute-start(bf16[80,1024]{1,0:T(8,128)(2,1)} %get-tuple-element.99), channel_id=1, source_target_pairs={{0,16},{2,18},{4,20},{6,22},{8,24},{10,26},{12,28},{14,30},{16,0},... | collective-permute-start | bytes 491528 | tf_op jit(solution)/shard_map/ppermute | solution.py:33
  170.9 20.7 %collective-permute-start.32 = (bf16[80,1024]{1,0:T(8,128)(2,1)}, bf16[80,1024]{1,0:T(8,128)(2,1)S(1)}, u32[]{:S(2)}, u32[]{:S(2)}) collective-permute-start(bf16[80,1024]{1,0:T(8,128)(2,1)} %get-tuple-element.100), channel_id=1, source_target_pairs={{0,24},{2,26},{4,28},{6,30},{8,16},{10,18},{12,20},{14,22},{16,8},... | collective-permute-start | bytes 491528 | tf_op jit(solution)/shard_map/ppermute | solution.py:33
  190.0 22.4 %collective-permute-start.29 = (bf16[256,1024]{1,0:T(8,128)(2,1)}, bf16[256,1024]{1,0:T(8,128)(2,1)S(1)}, u32[]{:S(2)}, u32[]{:S(2)}) collective-permute-start(bf16[256,1024]{1,0:T(8,128)(2,1)} %unfolded.3.refs_1_.held_ref), channel_id=1, source_target_pairs={{0,8},{2,18},{4,12},{6,22},{8,0},{10,26},{12,4},{14,30},{16,24},{1... | collective-permute-start | bytes 1572872 | tf_op jit(solution)/shard_map/ppermute | solution.py:112
  192.6 19.8 %copy-start.20 = (bf16[80,1024]{1,0:T(8,128)(2,1)}, bf16[80,1024]{1,0:T(8,128)(2,1)S(1)}, u32[]{:S(2)}) copy-start(bf16[80,1024]{1,0:T(8,128)(2,1)S(1)} %pad_maximum_fusion.4.rest_0_) | copy-start | bytes 491524
  192.6 13.4 %collective-permute-start.35 = (bf16[80,1024]{1,0:T(8,128)(2,1)S(1)}, bf16[80,1024]{1,0:T(8,128)(2,1)S(1)}, u32[]{:S(2)}, u32[]{:S(2)}) collective-permute-start(bf16[80,1024]{1,0:T(8,128)(2,1)S(1)} %pad_maximum_fusion.4.rest_0_), channel_id=1, source_target_pairs={{0,16},{2,18},{4,20},{6,22},{8,24},{10,26},{12,28},{14,30},{16,0},... | collective-permute-start | bytes 491528 | tf_op jit(solution)/shard_map/ppermute | solution.py:33
  198.1 10.2 %collective-permute-start.34 = (bf16[80,1024]{1,0:T(8,128)(2,1)S(1)}, bf16[80,1024]{1,0:T(8,128)(2,1)S(1)}, u32[]{:S(2)}, u32[]{:S(2)}) collective-permute-start(bf16[80,1024]{1,0:T(8,128)(2,1)S(1)} %pad_maximum_fusion.4.rest_0_), channel_id=1, source_target_pairs={{0,24},{2,26},{4,28},{6,30},{8,16},{10,18},{12,20},{14,22},{16,8},... | collective-permute-start | bytes 491528 | tf_op jit(solution)/shard_map/ppermute | solution.py:33
  199.1 17.5 %collective-permute-start.36 = (bf16[80,1024]{1,0:T(8,128)(2,1)S(1)}, bf16[80,1024]{1,0:T(8,128)(2,1)S(1)}, u32[]{:S(2)}, u32[]{:S(2)}) collective-permute-start(bf16[80,1024]{1,0:T(8,128)(2,1)S(1)} %pad_maximum_fusion.4.rest_0_), channel_id=1, source_target_pairs={{0,8},{2,10},{4,12},{6,14},{8,0},{10,2},{12,4},{14,6},{16,24},{18,... | collective-permute-start | bytes 491528 | tf_op jit(solution)/shard_map/ppermute | solution.py:33
  215.4 15.0 %collective-permute-start.33 = (bf16[512,1024]{1,0:T(8,128)(2,1)}, bf16[512,1024]{1,0:T(8,128)(2,1)S(1)}, u32[]{:S(2)}, u32[]{:S(2)}) collective-permute-start(bf16[512,1024]{1,0:T(8,128)(2,1)} %unfolded.4.refs_1_.held_ref), channel_id=1, source_target_pairs={{0,4},{2,10},{4,0},{6,14},{8,12},{10,2},{12,8},{14,6},{16,20},{18,... | collective-permute-start | bytes 3145736 | tf_op jit(solution)/shard_map/ppermute | solution.py:112
  219.3 2.3 collective-permute-start.37
  221.6 8.8 %copy-start.5 = (bf16[320,1024]{1,0:T(8,128)(2,1)}, bf16[320,1024]{1,0:T(8,128)(2,1)S(1)}, u32[]{:S(2)}) copy-start(bf16[320,1024]{1,0:T(8,128)(2,1)S(1)} %collective-permute-done.37.rest_0_.second_ref.rest_1_) | copy-start | bytes 1966084
  234.4 4.4 %collective-permute-start.38 = (bf16[1024,1024]{1,0:T(8,128)(2,1)}, bf16[1024,1024]{1,0:T(8,128)(2,1)S(1)}, u32[]{:S(2)}, u32[]{:S(2)}) collective-permute-start(bf16[1024,1024]{1,0:T(8,128)(2,1)} %unfolded.5.own_ref.own_gate), channel_id=1, source_target_pairs={{0,2},{2,0},{4,6},{6,4},{8,10},{10,8},{12,14},{14,12},{16,18},{18,... | collective-permute-start | bytes 6291464 | tf_op jit(solution)/shard_map/ppermute | solution.py:33
  234.4 17.5 %collective-permute-start.39 = (bf16[320,1024]{1,0:T(8,128)(2,1)}, bf16[320,1024]{1,0:T(8,128)(2,1)}, u32[]{:S(2)}, u32[]{:S(2)}) collective-permute-start(bf16[320,1024]{1,0:T(8,128)(2,1)} %pad_maximum_fusion.first_ref.rest_0_), channel_id=1, source_target_pairs={{0,4},{2,6},{4,0},{6,2},{8,12},{10,14},{12,8},{14,10},{16,20},{18,... | collective-permute-start | bytes 1966088 | tf_op jit(solution)/shard_map/ppermute | solution.py:33
  249.6 2.3 copy-start.44
  249.6 3.0 %copy-start.4 = (f32[256,1024]{1,0:T(8,128)S(1)}, f32[256,1024]{1,0:T(8,128)}, u32[]{:S(2)}) copy-start(f32[256,1024]{1,0:T(8,128)} %copy-done.3) | copy-start | bytes 3145732
  249.6 3.0 %copy-start.10 = (bf16[256,512]{1,0:T(8,128)(2,1)S(1)}, bf16[256,512]{1,0:T(8,128)(2,1)}, u32[]{:S(2)}) copy-start(bf16[256,512]{1,0:T(8,128)(2,1)} %own_ref.1) | copy-start | bytes 786436
  249.6 3.0 %copy-start.12 = (f32[256,512]{1,0:T(8,128)S(1)}, f32[256,512]{1,0:T(8,128)}, u32[]{:S(2)}) copy-start(f32[256,512]{1,0:T(8,128)} %copy-done.11) | copy-start | bytes 1572868
  249.6 3.0 %copy-start.46 = (f32[256]{0:T(256)S(1)}, f32[256]{0:T(256)}, u32[]{:S(2)}) copy-start(f32[256]{0:T(256)} %get-tuple-element.113) | copy-start | bytes 3076
  251.9 2.8 %collective-permute-start.40 = (bf16[320,1024]{1,0:T(8,128)(2,1)}, bf16[320,1024]{1,0:T(8,128)(2,1)S(1)}, u32[]{:S(2)}, u32[]{:S(2)}) collective-permute-start(bf16[320,1024]{1,0:T(8,128)(2,1)} %after.9.first_ref.rest_2_), channel_id=1, source_target_pairs={{0,2},{2,0},{4,6},{6,4},{8,10},{10,8},{12,14},{14,12},{16,18},{18,... | collective-permute-start | bytes 1966088 | tf_op jit(solution)/shard_map/ppermute | solution.py:33
  255.5 6.4 %copy-start.1 = (bf16[1024,1024]{1,0:T(8,128)(2,1)S(1)}, bf16[1024,1024]{1,0:T(8,128)(2,1)}, u32[]{:S(2)}) copy-start(bf16[1024,1024]{1,0:T(8,128)(2,1)} %param.23) | copy-start | bytes 6291460
  (25 other events, 19.6 us)

commit v13 on v12

--- a/solution.py
+++ b/solution.py
@@ -478,6 +478,7 @@
     returning_ref,
     skip_ref,
     step_weight_ref,
+    earlier_ref,
     first_wait,
     second_wait,
     act_grad_ref,
@@ -517,12 +518,6 @@
     small_ref[rank + count : rank + count + 1, :] = jnp.sum(grads * act, axis=0, keepdims=True)
     states[:count, :] = entry_ref[...]
 
-    @pl.when(pl.program_id(0) == 0)
-    def _():
-        in_sum[...] = jnp.zeros(in_sum.shape, f32)
-        read_sum[...] = jnp.zeros(read_sum.shape, f32)
-        select_grad_ref[...] = jnp.zeros(select_grad_ref.shape, f32)
-
     def forward(block, state):
         columns = coef_columns(coef, block)
         for i in range(body_rows):
@@ -546,8 +541,8 @@
             here = at_token(t, count)
             grad = scan_grad[row, :]
             summed = columns[count:, i : i + 1] * grad + adjoint
-            read_sum[here, :] += tree_sum(lane_tiles(grad * states[at_token(t + 1, count), :]))
-            in_sum[here, :] += tree_sum(lane_tiles(summed * drive[row, :]))
+            read_sum[here, :] = tree_sum(lane_tiles(grad * states[at_token(t + 1, count), :]))
+            in_sum[here, :] = tree_sum(lane_tiles(summed * drive[row, :]))
             keep_halves(halves, i, summed * columns[:count, i : i + 1])
             adjoint = factors[here, :] * summed
             held = adjoint * states[here, :]
@@ -567,19 +562,18 @@
     small_ref[rank : rank + count, :] = decay_grad * decay
     bias_grad = jnp.sum(pre_grad.astype(f32), axis=0, keepdims=True)
     small_ref[rank + count + 1 : rank + count + 2, :] = bias_grad
-    select_grad_ref[:rank, :] += lax.dot_general(
+    select_grad_ref[:rank, :] = earlier_ref[:rank, :] + lax.dot_general(
         step_weight_ref[...], pre_grad, contract_last, preferred_element_type=f32
     )
-
-    @pl.when(pl.program_id(0) == pl.num_programs(0) - 1)
-    def _():
-        for n in range(count):
-            at = pl.ds(n, rows, stride=count)
-            select_grad_ref[rank + n : rank + n + 1, :] = lane_sums(in_sum[at, :])
-            select_grad_ref[rank + count + n : rank + count + n + 1, :] = lane_sums(read_sum[at, :])
+    for n in range(count):
+        at = pl.ds(n, rows, stride=count)
+        for sums, start in ((in_sum, rank), (read_sum, rank + count)):
+            row = slice(start + n, start + n + 1)
+            select_grad_ref[row, :] = earlier_ref[row, :] + lane_sums(sums[at, :])
 
 
 def scan_backward(
+    part,
     selected,
     other,
     step_pre,
@@ -594,9 +588,10 @@
     returning,
     skip_gain,
     step_weight,
+    earlier,
     waits,
 ):
-    rows, width = step.shape
+    rows, width = step.shape[0], scan_width
     count = decay_log.shape[0]
     columns = selected.shape[0]
     rank = step_weight.shape[0]
@@ -609,18 +604,19 @@
         [
             whole_spec(columns, rows),
             whole_spec(columns, rows),
-            column_spec(rows),
-            column_spec(rows),
-            column_spec(rows),
-            part_spec(1, rows),
-            column_spec(rows),
+            column_spec(rows, part),
+            column_spec(rows, part),
+            column_spec(rows, part),
+            part_spec(1, rows, part),
+            column_spec(rows, part),
             whole_spec(rows, masks.shape[1]),
-            column_spec(count),
-            column_spec(count),
-            column_spec(2 * count + 8),
-            column_spec(count),
-            column_spec(1),
-            column_spec(rank),
+            column_spec(count, part),
+            column_spec(count, part),
+            column_spec(2 * count + 8, part),
+            column_spec(count, part),
+            column_spec(1, part),
+            column_spec(rank, part),
+            whole_spec(columns, rows),
         ]
         + [pl.BlockSpec(memory_space=pl.ANY)] * 2,
         [column_spec(rows), whole_spec(columns, rows), column_spec(small)],
@@ -653,6 +649,7 @@
         returning,
         skip_gain,
         step_weight,
+        earlier,
         *waits,
     )
 
@@ -661,7 +658,8 @@
     select_grad_ref,
     other_ref,
     select_ref,
-    act_grad_ref,
+    first_act_grad,
+    second_act_grad,
     convolved_ref,
     act_ref,
     inner_ref,
@@ -674,7 +672,8 @@
     taps = conv_weight_ref.shape[0]
     columns = select_ref.shape[0]
     select_grad = (select_grad_ref[...] + other_ref[...]).astype(bf16)
-    total = act_grad_ref[...] + lax.dot_general(
+    act_grad = jnp.where(pl.program_id(0) == 0, first_act_grad[...], second_act_grad[...])
+    total = act_grad + lax.dot_general(
         select_grad, select_ref[...], contract_first, preferred_element_type=f32
     )
     conv_grad = total * silu_slope(convolved_ref[...])
@@ -706,7 +705,7 @@
 
 
 def convolve_grad(
-    select_grad, other, select_weight, act_grad, convolved, act, projected, conv_weight, masks, waits
+    select_grad, other, select_weight, act_grads, convolved, act, projected, conv_weight, masks, waits
 ):
     rows, width = act.shape
     extended = rows + halo
@@ -721,7 +720,8 @@
             whole_spec(columns, rows),
             whole_spec(columns, rows),
             column_spec(columns),
-            column_spec(rows),
+            whole_spec(rows, scan_width),
+            whole_spec(rows, scan_width),
             column_spec(rows),
             column_spec(rows),
             part_spec(0, extended),
@@ -740,7 +740,7 @@
         select_grad,
         other,
         select_weight,
-        act_grad,
+        *act_grads,
         convolved,
         act,
         projected,
@@ -878,11 +878,13 @@
 block_rows, used_rows = 16, 12
 
 
-def small_kernel(place_ref, scan_ref, conv_ref, wait_ref, keep_ref, *rest):
+def small_kernel(place_ref, first_scan, second_scan, conv_ref, wait_ref, keep_ref, *rest):
     *sends_refs, rows, blocks = rest
     rows[...] = jnp.zeros(rows.shape, f32)
-    rows[: scan_ref.shape[0], :] = scan_ref[...]
-    rows[scan_ref.shape[0] : scan_ref.shape[0] + conv_ref.shape[0], :] = conv_ref[...]
+    count = first_scan.shape[0]
+    rows[:count, :scan_width] = first_scan[...]
+    rows[:count, scan_width:] = second_scan[...]
+    rows[count : count + conv_ref.shape[0], :] = conv_ref[...]
     blocks[...] = jnp.zeros(blocks.shape, f32)
     for n in range(16):
         blocks[n * block_rows : n * block_rows + used_rows, :] = rows[
@@ -898,12 +900,12 @@
             sends_refs[n - 1][...] = block.astype(bf16)
 
 
-def small_quarters(place, scan_small, conv_small, wait):
-    width = scan_small.shape[1]
+def small_quarters(place, scan_smalls, conv_small, wait):
+    width = conv_small.shape[1]
     return pl.pallas_call(
         small_kernel,
         in_specs=[pl.BlockSpec(memory_space=pltpu.SMEM)]
-        + [pl.BlockSpec(memory_space=pltpu.VMEM)] * 2
+        + [pl.BlockSpec(memory_space=pltpu.VMEM)] * 3
         + [pl.BlockSpec(memory_space=pl.ANY)],
         out_shape=[jax.ShapeDtypeStruct((4 * block_rows, width), f32)]
         + [jax.ShapeDtypeStruct((4 * block_rows, width), bf16)] * 3,
@@ -913,7 +915,7 @@
         ],
         cost_estimate=tiny_cost,
         name="small_quarters",
-    )(place, scan_small, conv_small, wait)
+    )(place, *scan_smalls, conv_small, wait)
 
 
 def quarter_kernel(
@@ -1076,7 +1078,8 @@
     )
 
 
-def early_send_kernel(core_ref, gated_ref, cot_ref, normed_ref, gate_grad_ref, out_ref, *, waits):
+def early_send_kernel(core_ref, gated_ref, cot_ref, normed_ref, gate_grad_ref, *rest, waits):
+    out_ref = rest[waits]
     size = out_ref.shape[0] // 2
     for core, left, right in ((1, gated_ref, cot_ref), (0, normed_ref, gate_grad_ref)):
 
@@ -1153,22 +1156,23 @@
     )
 
 
-def widen_kernel(place_ref, own_ref, other_ref, out_ref):
+def widen_kernel(place_ref, own_ref, other_ref, wait_ref, out_ref):
     out_ref[...] = jnp.where(place_ref[0] & 1 == 1, other_ref[...], own_ref[...]).astype(f32)
 
 
-def widened(place, own, other):
+def widened(place, own, other, wait):
     rows, width = own.shape
     block = pl.BlockSpec((rows // 4, width), lambda j: (j, 0))
     return pl.pallas_call(
         widen_kernel,
         grid=(4,),
-        in_specs=[pl.BlockSpec(memory_space=pltpu.SMEM), block, block],
+        in_specs=[pl.BlockSpec(memory_space=pltpu.SMEM), block, block]
+        + [pl.BlockSpec(memory_space=pl.ANY)],
         out_specs=block,
         out_shape=jax.ShapeDtypeStruct((rows, width), f32),
         cost_estimate=tiny_cost,
         name="widened",
-    )(place, own, other)
+    )(place, own, other, wait)
 
 
 def through(decay, total):
@@ -1310,7 +1314,12 @@
     factors = [gated, cot_whole, normed, gate_grad]
     size, depth = out_weight.shape[0], cot_whole.shape[1]
     send = small_call(
-        early_send_kernel, "early_send", jax.ShapeDtypeStruct((size, depth), bf16), [core], factors, []
+        early_send_kernel,
+        "early_send",
+        jax.ShapeDtypeStruct((size, depth), bf16),
+        [core],
+        factors,
+        [returning],
     )
     arrived = swapped(send, "wide", 1)
     out_part = jnp.dot(gated, out_weight, preferred_element_type=f32)
@@ -1321,34 +1330,45 @@
         [jax.ShapeDtypeStruct((size // 2, depth), kind) for kind in (f32, bf16)],
         [core, early_upper(steps[0])],
         [*factors, arrived],
-        [out_other, returning],
+        [out_other],
     )
     arrived = early_swapped(send, steps[0])
     out_theirs = swapped(out_other, "narrow", 1)
-    act_grad, select_grad, scan_small = scan_backward(
-        selected,
-        other_selected,
-        step_pre,
-        step,
-        act,
-        projected,
-        gated_grad,
-        masks,
-        decay_log,
-        entry,
-        passed,
-        returning,
-        skip_gain[None],
-        step_weight,
-        [send, out_other],
-    )
+    select_grad = jnp.zeros(selected.shape, f32)
+    waits, act_grads, scan_smalls = [send, out_other], [], []
+    for part in range(2):
+        act_grad, select_grad, scan_small = scan_backward(
+            part,
+            selected,
+            other_selected,
+            step_pre,
+            step,
+            act,
+            projected,
+            gated_grad,
+            masks,
+            decay_log,
+            entry,
+            passed,
+            returning,
+            skip_gain[None],
+            step_weight,
+            select_grad,
+            waits,
+        )
+        act_grads.append(act_grad)
+        scan_smalls.append(scan_small)
+        if part == 0:
+            early, send = folded(early, arrived, steps[1], select_grad)
+            arrived = early_swapped(send, steps[1])
+            waits = [send, out_other]
     layer_out = (tokens.astype(f32) + (out_mine + out_theirs)).astype(bf16)
     normed_four = quarter_of_four(after(normed, select_grad))
     inner_main, before, last, conv_small = convolve_grad(
         select_grad,
         swapped(select_grad, "narrow", 1),
         select_weight,
-        act_grad,
+        act_grads,
         convolved,
         act,
         projected,
@@ -1357,12 +1377,13 @@
         [out_theirs],
     )
     following = passed_along(before, "wide", -1)
-    early, send = folded(early, arrived, steps[1], conv_small)
-    arrived = early_swapped(send, steps[1])
-    inner_grad = patched(segment_ids, inner_main, last, following, send, *normed_four)
+    for bits in steps[2:]:
+        early, send = folded(early, arrived, bits, conv_small, *normed_four)
+        arrived = early_swapped(send, bits)
+    inner_grad = patched(segment_ids, inner_main, last, following, send)
     near = swapped(inner_grad, "wide", 2)
     far = swapped(inner_grad, "wide", 1)
-    keep, *sends = small_quarters(four_place, scan_small, conv_small, inner_grad)
+    keep, *sends = small_quarters(four_place, scan_smalls, conv_small, inner_grad)
     smalls = [keep] + [swapped(sends[n - 1], "wide", n) for n in (1, 2, 3)]
     normed_part = jnp.einsum(
         "cte,dce->td", jnp.stack([inner_grad, gate_grad]), in_weight, preferred_element_type=f32
@@ -1372,16 +1393,16 @@
     gain_sum = gain_part + swapped(gain_part, "narrow", 1)
     for bit in (bit for bits in more_bits for bit in bits):
         gain_sum = gain_sum + swapped(gain_sum, "wide", bit)
-    for bits in steps[2:]:
-        early, send = folded(early, arrived, bits, gain_part, *sends)
-        arrived = early_swapped(send, bits)
+    early = settled(early, arrived, gain_part, *sends)
+    for bits in steps[:1:-1]:
+        back = early_swapped(early, bits)
+        early = unfolded(early, back, bits, *smalls[1:])
+    back = early_swapped(early, steps[1])
     normed_mine, normed_other = narrow_halves(normed_part)
     row_theirs = swapped(row_part, "narrow", 1)
     normed_theirs = swapped(normed_other, "narrow", 1)
-    near = after(near, send, gain_sum, row_theirs, *smalls[1:])
+    near = after(near, early, gain_sum, row_theirs, *smalls[1:])
     last = swapped(near, "wide", 1)
-    early = settled(early, arrived, near)
-    back = early_swapped(early, steps[-1])
     keep, *sends = inner_quarter(
         (wide_place >> 2 & 3)[None],
         inner_grad,
@@ -1390,11 +1411,8 @@
         last,
         normed_four,
         smalls,
-        [early],
-    )
-    for bits, following_bits in zip(steps[:1:-1], steps[-2:0:-1]):
-        early = unfolded(early, back, bits, keep)
-        back = early_swapped(early, following_bits)
+        [],
+    )
     row_sum = (row_part + row_theirs).reshape(rows, 1)
     gain_mine = jnp.where(right_half, norm_gain[features:], norm_gain[:features])
     whole_grad = inverse * (gain_mine * (normed_mine + normed_theirs)) - tokens.astype(f32) * (
@@ -1402,7 +1420,7 @@
     ) * (row_sum / (2 * features))
     tokens_grad = (whole_grad + cotangent.astype(f32)).astype(bf16)
     arrived = [swapped(sends[n - 1], "wide", flips(first_bits)[n]) for n in (1, 2, 3)]
-    arrived[0] = after(arrived[0], early, normed_theirs)
+    arrived[0] = after(arrived[0], normed_theirs)
     held = keep + sum(a.astype(f32) for a in arrived)
     for bits in more_bits:
         held = scattered(held, bits)
@@ -1412,14 +1430,15 @@
     spare = jnp.broadcast_to(gain_sum, (block_rows - used_rows, gain_sum.shape[1]))
     held = jnp.concatenate([held[: held.shape[0] - spare.shape[0]], spare.astype(bf16)])
     early = unfolded(early, back, steps[1], held)
-    back = early_swapped(early, steps[0])
+    early = unfolded(early, early_swapped(early, steps[0]), steps[0])
     held = gathered(held, first_bits, early)
+    core_early = swapped(early, "wide", 1)
     core = swapped(held, "wide", 1)
-    early = unfolded(early, back, steps[0], core)
-    core_early = swapped(early, "wide", 1)
-    out_weight_grad = widened(four_place, early, core_early)
+    out_weight_grad = widened(four_place, early, core_early, core)
     gates = (early, core_early)
-    (begun,) = joined(four_place, 0, gates, held, core, (), (out_weight_grad,))
+    (begun,) = joined(
+        four_place, 0, gates, held, core, (), (layer_out, tokens_grad, out_weight_grad)
+    )
     near = after(swapped(held, "wide", 2), begun)
     far = swapped(near, "wide", 1)
     conv_at = rank + count + 2

time: 263 us -> 275 us (1.046)
  Pallas kernels: 107 us -> 111 us
  starting transfers between devices: 50.9 us -> 54 us
    ppermute x30, waiting for transfers between devices: 28.3 us -> 46.7 us  [swapped(): return lax.ppermute(array, axis, [(i, i ^ bit) for i in range(peers)])]
    ppermute x6, waiting for transfers between devices: 29.5 us -> 16.4 us  [early_swapped(): lax.ppermute(array, 'wide', [(i, i ^ bits[i % 2]) for i in range(peers)])]
    ppermute x4, waiting for transfers between devices: 4.31 us -> 0.03 us  [passed_along(): return lax.ppermute(array, axis, pairs)]
    pallas_call x5 -> x6, Pallas kernels: 53.6 us -> 57.4 us  [call(): pl.pallas_call(kernel, grid=(width // scan_width,), in_specs=in_specs, ou...]
    ppermute x6, starting transfers between devices: 5.98 us -> 9.44 us  [early_swapped(): lax.ppermute(array, 'wide', [(i, i ^ bits[i % 2]) for i in range(peers)])]
    unnamed x96 -> x106, local copies, waits for them, and re-layouts: 13.3 us -> 15.4 us
  transfers between devices with their start and end apart: 41 -> 41, of which waited for: 17 -> 16; matrix products, arithmetic and copies ran while one was open for 10% -> 10% of each run, Pallas kernels for 25% -> 28%
where the time goes in v13:
time: 275 us; the launch traced here: 273 us
  Pallas kernels  111 us (40%)
  waiting for transfers between devices  63.1 us (23%)
  starting transfers between devices  54 us (20%)
  local copies, waits for them, and re-layouts  18.5 us (7%)
  matrix products  12.4 us (5%)
  other arithmetic  12.4 us (5%)
    pallas_call x6, Pallas kernels, call(): pl.pallas_call(kernel, grid=(width // scan_width,), in_specs=in_specs, ou...  57.4 us
    ppermute x30, waiting for transfers between devices, swapped(): return lax.ppermute(array, axis, [(i, i ^ bit) for i in range(peers)])  46.7 us
    ppermute x30, starting transfers between devices, swapped(): return lax.ppermute(array, axis, [(i, i ^ bit) for i in range(peers)])  31.8 us
    pallas_call x8, Pallas kernels, small_call(): pl.pallas_call(functools.partial(kernel, waits=len(waits)), in_specs=[pl....  23.3 us
    ppermute x6, waiting for transfers between devices, early_swapped(): lax.ppermute(array, 'wide', [(i, i ^ bits[i % 2]) for i in range(peers)])  16.4 us
    unnamed x106, local copies, waits for them, and re-layouts  15.4 us
    ppermute x4, starting transfers between devices, passed_along(): return lax.ppermute(array, axis, pairs)  11.3 us
    pallas_call x2, Pallas kernels, joined(): pl.pallas_call(functools.partial(join_kernel, small_rows=small_rows), gri...  11.2 us
  transfers between devices with their start and end apart: 41, of which 16 were waited for; matrix products, arithmetic and copies ran while one was open for 10% of the time, Pallas kernels for 28%

profile of v13, /device:TPU:0, one launch (start us, length us, event | category | flops | bytes accessed | tf_op | source)
XLA Modules:
  0.0 273.2 jit_solution(6859949466962615765)
XLA Ops:
  0.7 3.0 %collective-permute-start = (bf16[256,512]{1,0:T(8,128)(2,1)}, bf16[256,512]{1,0:T(8,128)(2,1)S(1)}, u32[]{:S(2)}, u32[]{:S(2)}) collective-permute-start(bf16[256,512]{1,0:T(8,128)(2,1)} %own_ref.1), channel_id=1, source_target_pairs={{0,1},{1,0},{2,3},{3,2},{4,5},{5,4},{6,7},{7,6},{8,9},{9,8},{10,11... | collective-permute-start | bytes 786440 | tf_op jit(solution)/shard_map/ppermute | solution.py:33
  3.7 1.4 edge_rows.1
  5.1 1.4 collective-permute-start.2
  6.5 4.0 %collective-permute-start.1 = (bf16[16,512]{1,0:T(8,128)(2,1)}, bf16[16,512]{1,0:T(8,128)(2,1)S(1)}, u32[]{:S(2)}, u32[]{:S(2)}) collective-permute-start(bf16[16,512]{1,0:T(8,128)(2,1)} %edge_rows.1), channel_id=1, source_target_pairs={{0,2},{2,4},{4,6},{6,8},{8,10},{10,12},{12,14},{14,16},{16,18},{18... | collective-permute-start | bytes 49160 | tf_op jit(solution)/shard_map/ppermute | solution.py:28
  10.5 1.5 collective-permute-start.4
  12.8 2.5 normalized.1
  15.3 4.9 %fusion.7.inner_ref.gate_ref = bf16[2,272,1024]{2,1,0:T(8,128)(2,1)} fusion(bf16[1024,2,1024]{2,1,0:T(2,128)(2,1)} %param.15, bf16[272,1024]{1,0:T(8,128)(2,1)} %get-tuple-element.64), kind=kOutput, calls=%fused_computation.5 | convolution fusion | flops 1141407744 | bytes 5865472 | tf_op jit(solution)/shard_map/td,dce->cte/dot_general | solution.py:1267
  20.2 3.5 %convolve.1 = (f32[256,1024]{1,0:T(8,128)}, bf16[256,1024]{1,0:T(8,128)(2,1)}, f32[96,256]{1,0:T(8,128)}) custom-call(bf16[2,272,1024]{2,1,0:T(8,128)(2,1)} %fusion.7.inner_ref.gate_ref, f32[4,1024]{1,0:T(4,128)} %conv_weight_ref.3, f32[1,1024]{1,0:T(1,128)} %bitcast.42, bf16[96,1024]{1,0:T(8,128)(2,1)} %select_ref.3, f32[256,128]{1,0:T(8,128)} %get-tuple-element.65.mask_ref), custom_call_target="tpu_custom_call" | custom-call | flops 1 | bytes 1 | tf_op jit(solution)/shard_map/convolve/pallas_call | solution.py:147
  24.8 1.8 fusion.28.gated_grad_ref
  26.6 2.1 collective-permute-done.3.other_ref
  29.3 10.7 %scan_ends.1 = (f32[256,1024]{1,0:T(8,128)}, f32[256,1024]{1,0:T(8,128)}, f32[40,1024]{1,0:T(8,128)}) custom-call(f32[96,256]{1,0:T(8,128)} %get-tuple-element.66.selected_ref, f32[96,256]{1,0:T(8,128)} %copy-done.16, bf16[64,1024]{1,0:T(8,128)(2,1)} %step_weight_ref.5, f32[1,1024]{1,0:T(1,128)} %bitcast.43, bf16[256,1024]{1,0:T(8,128)(2,1)} %get-tuple-element.67.act_ref, ...), custom_call_target="tpu_custom_call" | custom-call | flops 1 | bytes 1 | tf_op jit(solution)/shard_map/scan_ends/pallas_call | solution.py:147
  40.1 1.6 collective-permute-done.5.other_ref
  42.4 1.9 carry_round.2
  44.3 1.7 collective-permute-start.6
  46.0 4.8 %collective-permute-done.6.other_ref = f32[40,1024]{1,0:T(8,128)S(1)} collective-permute-done((f32[40,1024]{1,0:T(8,128)}, f32[40,1024]{1,0:T(8,128)S(1)}, u32[]{:S(2)}, u32[]{:S(2)}) %collective-permute-start.6) | collective-permute-done | bytes 163872 | tf_op jit(solution)/shard_map/ppermute | solution.py:33
  51.4 1.9 carry_round.3
  53.2 4.6 %collective-permute-start.7 = (f32[16,1024]{1,0:T(8,128)}, f32[16,1024]{1,0:T(8,128)S(1)}, u32[]{:S(2)}, u32[]{:S(2)}) collective-permute-start(f32[16,1024]{1,0:T(8,128)} %get-tuple-element.73), channel_id=1, source_target_pairs={{0,8},{2,10},{4,12},{6,14},{8,16},{10,18},{12,20},{14,22},{16,24},... | collective-permute-start | bytes 196616 | tf_op jit(solution)/shard_map/ppermute | solution.py:28
  57.8 1.3 collective-permute-start.9
  60.7 10.4 %scan_forward.1 = (bf16[256,1024]{1,0:T(8,128)(2,1)}, bf16[256,1024]{1,0:T(8,128)(2,1)}, f32[16,1024]{1,0:T(8,128)}) custom-call(f32[96,256]{1,0:T(8,128)} %get-tuple-element.66.selected_ref, f32[96,256]{1,0:T(8,128)} %copy-done.16, f32[256,1024]{1,0:T(8,128)} %get-tuple-element.68.step_ref, bf16[256,1024]{1,0:T(8,128)(2,1)} %get-tuple-element.67.act_ref, ...), custom_call_target="tpu_custom_call" | custom-call | flops 1 | bytes 1 | tf_op jit(solution)/shard_map/scan_forward/pallas_call | solution.py:147
  71.7 3.6 %early_send.1 = bf16[1024,1024]{1,0:T(8,128)(2,1)} custom-call(s32[1]{0:T(128)} %bitcast.9.core_ref, bf16[256,1024]{1,0:T(8,128)(2,1)} %get-tuple-element.74.gated_ref, bf16[256,1024]{1,0:T(8,128)(2,1)} %pad_maximum_fusion.1.cot_ref, bf16[256,1024]{1,0:T(8,128)(2,1)} %get-tuple-element.79.normed_ref.refs_0_, ...), custom_call_target="tpu_custom_call" | custom-call | flops 1 | bytes 1 | tf_op jit(solution)/shard_map/early_send/pallas_call | solution.py:1058
  75.3 1.7 fusion.30
  77.9 1.9 collective-permute-done.10.arrived_ref
  79.8 5.2 %early_first.1 = (f32[512,1024]{1,0:T(8,128)}, bf16[512,1024]{1,0:T(8,128)(2,1)}) custom-call(s32[1]{0:T(128)} %bitcast.9.core_ref, s32[1]{0:T(128)} %bitcast.10.upper_ref, bf16[256,1024]{1,0:T(8,128)(2,1)} %get-tuple-element.74.gated_ref, bf16[256,1024]{1,0:T(8,128)(2,1)} %pad_maximum_fusion.1.cot_ref, ...), custom_call_target="tpu_custom_call" | custom-call | flops 1 | bytes 1 | tf_op jit(solution)/shard_map/early_first/pallas_call | solution.py:1058
  85.6 1.5 collective-permute-start.8
  87.7 13.9 %scan_backward.2 = (f32[256,512]{1,0:T(8,128)}, f32[96,256]{1,0:T(8,128)}, f32[82,512]{1,0:T(8,128)}) custom-call(f32[96,256]{1,0:T(8,128)} %get-tuple-element.66.selected_ref, f32[96,256]{1,0:T(8,128)} %copy-done.16, f32[256,1024]{1,0:T(8,128)} %get-tuple-element.76.step_pre_ref, f32[256,1024]{1,0:T(8,128)} %get-tuple-element.68.step_ref, ...), custom_call_target="tpu_custom_call" | custom-call | flops 1 | bytes 1 | tf_op jit(solution)/shard_map/scan_backward/pallas_call | solution.py:147
  102.7 3.2 %folded.2 = (f32[256,1024]{1,0:T(8,128)}, bf16[256,1024]{1,0:T(8,128)(2,1)}) custom-call(s32[1]{0:T(128)} %bitcast.11.upper_ref, f32[512,1024]{1,0:T(8,128)} %get-tuple-element.83.keep_ref, bf16[512,1024]{1,0:T(8,128)(2,1)} %copy-done.21, f32[96,256]{1,0:T(8,128)} %get-tuple-element.82.rest_0_.earlier_ref), custom_call_target="tpu_custom_call" | custom-call | flops 1 | bytes 1 | tf_op jit(solution)/shard_map/folded/pallas_call | solution.py:1058
  105.8 2.6 collective-permute-start.14
  108.4 13.9 %scan_backward.3 = (f32[256,512]{1,0:T(8,128)}, f32[96,256]{1,0:T(8,128)}, f32[82,512]{1,0:T(8,128)}) custom-call(f32[96,256]{1,0:T(8,128)} %get-tuple-element.66.selected_ref, f32[96,256]{1,0:T(8,128)} %copy-done.16, f32[256,1024]{1,0:T(8,128)} %get-tuple-element.76.step_pre_ref, f32[256,1024]{1,0:T(8,128)} %get-tuple-element.68.step_ref, ...), custom_call_target="tpu_custom_call" | custom-call | flops 1 | bytes 1 | tf_op jit(solution)/shard_map/scan_backward/pallas_call | solution.py:147
  122.9 1.8 constant_dynamic-slice_fusion
  124.7 1.2 collective-permute-start.17
  128.6 4.9 %convolve_grad.1 = (bf16[256,1024]{1,0:T(8,128)(2,1)}, f32[8,1024]{1,0:T(8,128)}, f32[8,1024]{1,0:T(8,128)}, f32[101,1024]{1,0:T(8,128)}) custom-call(f32[96,256]{1,0:T(8,128)} %get-tuple-element.85.select_grad_ref.refs_1_, f32[96,256]{1,0:T(8,128)} %copy-done.42, bf16[96,1024]{1,0:T(8,128)(2,1)} %select_ref.3, f32[256,512]{1,0:T(8,128)} %get-tuple-element.86.first_act_grad, ...), custom_call_target="tpu_custom_call" | custom-call | flops 1 | bytes 1 | tf_op jit(solution)/shard_map/convolve_grad/pallas_call | solution.py:147
  133.5 1.5 collective-permute-start.13
  136.7 2.4 folded.3
  139.0 2.8 %collective-permute-start.20 = (bf16[128,1024]{1,0:T(8,128)(2,1)}, bf16[128,1024]{1,0:T(8,128)(2,1)S(1)}, u32[]{:S(2)}, u32[]{:S(2)}) collective-permute-start(bf16[128,1024]{1,0:T(8,128)(2,1)} %get-tuple-element.94.rest_0_), channel_id=1, source_target_pairs={{0,16},{2,6},{4,20},{6,2},{8,24},{10,14},{12,28},{14,10},{16,0},{1... | collective-permute-start | bytes 786440 | tf_op jit(solution)/shard_map/ppermute | solution.py:112
  142.4 1.5 patched.1.wait_ref.own_ref
  145.0 2.2 small_quarters.1
  147.2 4.0 %fusion.10 = f32[256,1024]{1,0:T(8,128)S(1)} fusion(bf16[1024,2,1024]{2,1,0:T(2,128)(2,1)} %param.15, bf16[1,256,1024]{2,1,0:T(8,128)(2,1)S(1)} %bitcast.33, bf16[1,256,1024]{2,1,0:T(8,128)(2,1)} %bitcast.32), kind=kOutput, calls=%fused_computation.6 | convolution fusion | flops 1074266112 | bytes 6291456 | tf_op jit(solution)/shard_map/cte,dce->td/dot_general | solution.py:1388
  153.0 1.9 settled.1.held_ref
  154.8 1.7 collective-permute-start.21
  157.9 2.4 collective-permute-done.27
  161.1 1.3 convert_reduce_fusion
  162.4 1.2 collective-permute-done.23.rest_1_.refs_5_.second_ref
  164.0 2.6 collective-permute-done.24.rest_2_.refs_6_.third_ref
  167.9 1.9 unfolded.3.refs_1_.held_ref
  171.5 1.3 collective-permute-start.18
  172.8 3.5 %inner_quarter.1 = (f32[80,1024]{1,0:T(8,128)}, bf16[80,1024]{1,0:T(8,128)(2,1)}, bf16[80,1024]{1,0:T(8,128)(2,1)}, bf16[80,1024]{1,0:T(8,128)(2,1)}) custom-call(s32[1]{0:T(128)} %bitcast.20.place_ref, bf16[256,1024]{1,0:T(8,128)(2,1)} %patched.1.wait_ref.own_ref, bf16[256,1024]{1,0:T(8,128)(2,1)} %after.6.near_ref, ...), custom_call_target="tpu_custom_call" | custom-call | flops 1 | bytes 1 | tf_op jit(solution)/shard_map/inner_quarter/pallas_call | solution.py:965
  178.1 2.6 collective-permute-start.32
  180.8 5.3 %collective-permute-done.18.refs_1_ = f32[256,512]{1,0:T(8,128)S(1)} collective-permute-done((f32[256,512]{1,0:T(8,128)}, f32[256,512]{1,0:T(8,128)S(1)}, u32[]{:S(2)}, u32[]{:S(2)}) %collective-permute-start.18) | collective-permute-done | bytes 524320 | tf_op jit(solution)/shard_map/ppermute | solution.py:33
  187.5 7.3 %collective-permute-done.31 = bf16[80,1024]{1,0:T(8,128)(2,1)S(1)} collective-permute-done((bf16[80,1024]{1,0:T(8,128)(2,1)}, bf16[80,1024]{1,0:T(8,128)(2,1)S(1)}, u32[]{:S(2)}, u32[]{:S(2)}) %collective-permute-start.31) | collective-permute-done | bytes 163872 | tf_op jit(solution)/shard_map/ppermute | solution.py:33
  196.6 3.1 %collective-permute-done.25.arrived_ref = bf16[256,1024]{1,0:T(8,128)(2,1)S(1)} collective-permute-done((bf16[256,1024]{1,0:T(8,128)(2,1)S(1)}, bf16[256,1024]{1,0:T(8,128)(2,1)S(1)}, u32[]{:S(2)}, u32[]{:S(2)}) %collective-permute-start.25) | collective-permute-done | bytes 524320 | tf_op jit(solution)/shard_map/ppermute | solution.py:112
  200.5 2.2 unfolded.4.held_ref
  202.7 1.7 collective-permute-start.33
  204.4 13.3 %collective-permute-done.33.arrived_ref = bf16[512,1024]{1,0:T(8,128)(2,1)S(1)} collective-permute-done((bf16[512,1024]{1,0:T(8,128)(2,1)}, bf16[512,1024]{1,0:T(8,128)(2,1)S(1)}, u32[]{:S(2)}, u32[]{:S(2)}) %collective-permute-start.33) | collective-permute-done | bytes 1048608 | tf_op jit(solution)/shard_map/ppermute | solution.py:112
  218.7 3.0 %unfolded.5.refs_1_.own_ref.own_gate = bf16[1024,1024]{1,0:T(8,128)(2,1)} custom-call(s32[1]{0:T(128)} %bitcast.10.upper_ref, bf16[512,1024]{1,0:T(8,128)(2,1)} %unfolded.4.held_ref, bf16[512,1024]{1,0:T(8,128)(2,1)} %copy-done.20), custom_call_target="tpu_custom_call" | custom-call | flops 1 | bytes 1 | tf_op jit(solution)/shard_map/unfolded/pallas_call | solution.py:1058
  221.7 5.3 %collective-permute-start.34 = (bf16[1024,1024]{1,0:T(8,128)(2,1)}, bf16[1024,1024]{1,0:T(8,128)(2,1)S(1)}, u32[]{:S(2)}, u32[]{:S(2)}) collective-permute-start(bf16[1024,1024]{1,0:T(8,128)(2,1)} %unfolded.5.refs_1_.own_ref.own_gate), channel_id=1, source_target_pairs={{0,2},{2,0},{4,6},{6,4},{8,10},{10,8},{12,14},{14,12},{16,18},{18,... | collective-permute-start | bytes 6291464 | tf_op jit(solution)/shard_map/ppermute | solution.py:33
  228.0 1.6 collective-permute-start.35
  230.5 10.4 %collective-permute-done.36 = bf16[80,1024]{1,0:T(8,128)(2,1)S(1)} collective-permute-done((bf16[80,1024]{1,0:T(8,128)(2,1)S(1)}, bf16[80,1024]{1,0:T(8,128)(2,1)S(1)}, u32[]{:S(2)}, u32[]{:S(2)}) %collective-permute-start.36) | collective-permute-done | bytes 163872 | tf_op jit(solution)/shard_map/ppermute | solution.py:33
  246.0 1.7 collective-permute-start.38
  248.9 1.3 copy-done.2
  250.2 4.7 %widened.1.rest_2_ = f32[1024,1024]{1,0:T(8,128)} custom-call(s32[1]{0:T(128)} %bitcast.18.place_ref, bf16[1024,1024]{1,0:T(8,128)(2,1)} %unfolded.5.refs_1_.own_ref.own_gate, bf16[1024,1024]{1,0:T(8,128)(2,1)} %copy-done.2, bf16[320,1024]{1,0:T(8,128)(2,1)} %collective-permute-done.39.wait_ref.second_ref.rest_1_), custom_call_target="tpu_custom_call" | custom-call | flops 1 | bytes 1 | tf_op jit(solution)/shard_map/widened/pallas_call | solution.py:1166
  254.9 4.8 %joined.2.refs_1_.rest_4_ = f32[1024,2,1024]{2,1,0:T(2,128)} custom-call(s32[1]{0:T(128)} %bitcast.18.place_ref, bf16[1024,1024]{1,0:T(8,128)(2,1)} %unfolded.5.refs_1_.own_ref.own_gate, bf16[1024,1024]{1,0:T(8,128)(2,1)} %copy-done.2, bf16[320,1024]{1,0:T(8,128)(2,1)} %pad_maximum_fusion.first_ref.rest_0_, ...), custom_call_target="tpu_custom_call" | custom-call | flops 1 | bytes 1 | tf_op jit(solution)/shard_map/joined/pallas_call | solution.py:1031
  259.7 3.8 %collective-permute-done.38.refs_0_ = bf16[320,1024]{1,0:T(8,128)(2,1)} collective-permute-done((bf16[320,1024]{1,0:T(8,128)(2,1)}, bf16[320,1024]{1,0:T(8,128)(2,1)}, u32[]{:S(2)}, u32[]{:S(2)}) %collective-permute-start.38) | collective-permute-done | bytes 655392 | tf_op jit(solution)/shard_map/ppermute | solution.py:33
  263.5 2.3 collective-permute-done.40.second_ref.rest_3_
  266.6 6.4 %joined.3 = (f32[1024,2,1024]{2,1,0:T(2,128)}, f32[64,1024]{1,0:T(8,128)}, f32[16,1024]{1,0:T(8,128)}, f32[1,1024]{1,0:T(1,128)}, f32[1,1024]{1,0:T(1,128)}, /*i...) custom-call(s32[1]{0:T(128)} %bitcast.18.place_ref, ...), custom_call_target="tpu_custom_call", output_to_operand_aliasing={{0}: (9, {})} | custom-call | flops 1 | bytes 1 | tf_op jit(solution)/shard_map/joined/pallas_call | solution.py:1031
  (177 shorter events, 38.6 us)
Async XLA Ops:
  0.6 24.2 %copy-start = (bf16[1024,1024]{1,0:T(8,128)(2,1)S(1)}, bf16[1024,1024]{1,0:T(8,128)(2,1)}, u32[]{:S(2)}) copy-start(bf16[1024,1024]{1,0:T(8,128)(2,1)} %param.23) | copy-start | bytes 6291460
  0.7 11.4 %collective-permute-start = (bf16[256,512]{1,0:T(8,128)(2,1)}, bf16[256,512]{1,0:T(8,128)(2,1)S(1)}, u32[]{:S(2)}, u32[]{:S(2)}) collective-permute-start(bf16[256,512]{1,0:T(8,128)(2,1)} %own_ref.1), channel_id=1, source_target_pairs={{0,1},{1,0},{2,3},{3,2},{4,5},{5,4},{6,7},{7,6},{8,9},{9,8},{10,11... | collective-permute-start | bytes 786440 | tf_op jit(solution)/shard_map/ppermute | solution.py:33
  5.1 7.0 %collective-permute-start.2 = (bf16[16,512]{1,0:T(8,128)(2,1)}, bf16[16,512]{1,0:T(8,128)(2,1)S(1)}, u32[]{:S(2)}, u32[]{:S(2)}) collective-permute-start(bf16[16,512]{1,0:T(8,128)(2,1)} %edge_rows.1), channel_id=1, source_target_pairs={{0,3},{1,2},{2,5},{3,4},{4,7},{5,6},{6,9},{7,8},{8,11},{9,10},{10,... | collective-permute-start | bytes 49160 | tf_op jit(solution)/shard_map/ppermute | solution.py:51
  6.5 5.5 %collective-permute-start.1 = (bf16[16,512]{1,0:T(8,128)(2,1)}, bf16[16,512]{1,0:T(8,128)(2,1)S(1)}, u32[]{:S(2)}, u32[]{:S(2)}) collective-permute-start(bf16[16,512]{1,0:T(8,128)(2,1)} %edge_rows.1), channel_id=1, source_target_pairs={{0,2},{2,4},{4,6},{6,8},{8,10},{10,12},{12,14},{14,16},{16,18},{18... | collective-permute-start | bytes 49160 | tf_op jit(solution)/shard_map/ppermute | solution.py:28
  10.5 14.3 %collective-permute-start.4 = (bf16[256,512]{1,0:T(8,128)(2,1)}, bf16[256,512]{1,0:T(8,128)(2,1)S(1)}, u32[]{:S(2)}, u32[]{:S(2)}) collective-permute-start(bf16[256,512]{1,0:T(8,128)(2,1)} %param.25), channel_id=1, source_target_pairs={{0,1},{1,0},{2,3},{3,2},{4,5},{5,4},{6,7},{7,6},{8,9},{9,8},{10,11... | collective-permute-start | bytes 786440 | tf_op jit(solution)/shard_map/ppermute | solution.py:33
  15.3 9.5 %copy-start.22 = (bf16[256,512]{1,0:T(8,128)(2,1)S(1)}, bf16[256,512]{1,0:T(8,128)(2,1)}, u32[]{:S(2)}) copy-start(bf16[256,512]{1,0:T(8,128)(2,1)} %param.25) | copy-start | bytes 786436
  23.7 4.9 %collective-permute-start.3 = (f32[96,256]{1,0:T(8,128)}, f32[96,256]{1,0:T(8,128)S(1)}, u32[]{:S(2)}, u32[]{:S(2)}) collective-permute-start(f32[96,256]{1,0:T(8,128)} %get-tuple-element.66.selected_ref), channel_id=1, source_target_pairs={{0,1},{1,0},{2,3},{3,2},{4,5},{5,4},{6,7},{7,6},{8,9},{9,8},{10,11... | collective-permute-start | bytes 294920 | tf_op jit(solution)/shard_map/ppermute | solution.py:33
  40.0 1.7 collective-permute-start.5
  44.3 6.5 %collective-permute-start.6 = (f32[40,1024]{1,0:T(8,128)}, f32[40,1024]{1,0:T(8,128)S(1)}, u32[]{:S(2)}, u32[]{:S(2)}) collective-permute-start(f32[40,1024]{1,0:T(8,128)} %get-tuple-element.70.own_ref), channel_id=1, source_target_pairs={{0,4},{2,6},{4,0},{6,2},{8,12},{10,14},{12,8},{14,10},{16,20},{18,... | collective-permute-start | bytes 491528 | tf_op jit(solution)/shard_map/ppermute | solution.py:33
  53.2 6.8 %collective-permute-start.7 = (f32[16,1024]{1,0:T(8,128)}, f32[16,1024]{1,0:T(8,128)S(1)}, u32[]{:S(2)}, u32[]{:S(2)}) collective-permute-start(f32[16,1024]{1,0:T(8,128)} %get-tuple-element.73), channel_id=1, source_target_pairs={{0,8},{2,10},{4,12},{6,14},{8,16},{10,18},{12,20},{14,22},{16,24},... | collective-permute-start | bytes 196616 | tf_op jit(solution)/shard_map/ppermute | solution.py:28
  57.8 13.2 %collective-permute-start.9 = (f32[16,1024]{1,0:T(8,128)}, f32[16,1024]{1,0:T(8,128)S(1)}, u32[]{:S(2)}, u32[]{:S(2)}) collective-permute-start(f32[16,1024]{1,0:T(8,128)} %get-tuple-element.78), channel_id=1, source_target_pairs={{8,0},{10,2},{12,4},{14,6},{16,8},{18,10},{20,12},{22,14},{24,16},... | collective-permute-start | bytes 196616 | tf_op jit(solution)/shard_map/ppermute | solution.py:28
  75.3 4.5 %collective-permute-start.10 = (bf16[1024,1024]{1,0:T(8,128)(2,1)}, bf16[1024,1024]{1,0:T(8,128)(2,1)}, u32[]{:S(2)}, u32[]{:S(2)}) collective-permute-start(bf16[1024,1024]{1,0:T(8,128)(2,1)} %early_send.1), channel_id=1, source_target_pairs={{0,2},{2,0},{4,6},{6,4},{8,10},{10,8},{12,14},{14,12},{16,18},{18,... | collective-permute-start | bytes 6291464 | tf_op jit(solution)/shard_map/ppermute | solution.py:33
  79.8 5.8 %copy-start.5 = (f32[256,512]{1,0:T(8,128)S(1)}, f32[256,512]{1,0:T(8,128)}, u32[]{:S(2)}) copy-start(f32[256,512]{1,0:T(8,128)} %slice_select_fusion.1.rest_0_.second_wait) | copy-start | bytes 1572868
  85.0 16.6 %collective-permute-start.11 = (bf16[512,1024]{1,0:T(8,128)(2,1)}, bf16[512,1024]{1,0:T(8,128)(2,1)S(1)}, u32[]{:S(2)}, u32[]{:S(2)}) collective-permute-start(bf16[512,1024]{1,0:T(8,128)(2,1)} %get-tuple-element.81.first_wait), channel_id=1, source_target_pairs={{0,4},{2,10},{4,0},{6,14},{8,12},{10,2},{12,8},{14,6},{16,20},{18,... | collective-permute-start | bytes 3145736 | tf_op jit(solution)/shard_map/ppermute | solution.py:112
  85.6 40.6 %collective-permute-start.8 = (f32[256,512]{1,0:T(8,128)S(1)}, f32[256,512]{1,0:T(8,128)S(1)}, u32[]{:S(2)}, u32[]{:S(2)}) collective-permute-start(f32[256,512]{1,0:T(8,128)S(1)} %copy-done.5), channel_id=1, source_target_pairs={{0,1},{1,0},{2,3},{3,2},{4,5},{5,4},{6,7},{7,6},{8,9},{9,8},{10,11... | collective-permute-start | bytes 1572872 | tf_op jit(solution)/shard_map/ppermute | solution.py:33
  105.8 30.0 %collective-permute-start.14 = (bf16[256,1024]{1,0:T(8,128)(2,1)}, bf16[256,1024]{1,0:T(8,128)(2,1)S(1)}, u32[]{:S(2)}, u32[]{:S(2)}) collective-permute-start(bf16[256,1024]{1,0:T(8,128)(2,1)} %get-tuple-element.84.first_wait), channel_id=1, source_target_pairs={{0,8},{2,18},{4,12},{6,22},{8,0},{10,26},{12,4},{14,30},{16,24},{1... | collective-permute-start | bytes 1572872 | tf_op jit(solution)/shard_map/ppermute | solution.py:112
  122.3 5.6 %collective-permute-start.12 = (f32[96,256]{1,0:T(8,128)}, f32[96,256]{1,0:T(8,128)S(1)}, u32[]{:S(2)}, u32[]{:S(2)}) collective-permute-start(f32[96,256]{1,0:T(8,128)} %get-tuple-element.85.select_grad_ref.refs_1_), channel_id=1, source_target_pairs={{0,1},{1,0},{2,3},{3,2},{4,5},{5,4},{6,7},{7,6},{8,9},{9,8},{10,11... | collective-permute-start | bytes 294920 | tf_op jit(solution)/shard_map/ppermute | solution.py:33
  124.7 11.1 %collective-permute-start.17 = (bf16[256,256]{1,0:T(8,128)(2,1)S(1)}, bf16[256,256]{1,0:T(8,128)(2,1)S(1)}, u32[]{:S(2)}, u32[]{:S(2)}) collective-permute-start(bf16[256,256]{1,0:T(8,128)(2,1)S(1)} %get-tuple-element.124), channel_id=1, source_target_pairs={{0,6},{2,4},{4,2},{6,0},{8,14},{10,12},{12,10},{14,8},{16,22},{18,... | collective-permute-start | bytes 393224 | tf_op jit(solution)/shard_map/ppermute | solution.py:33
  125.9 9.9 %collective-permute-start.16 = (bf16[256,256]{1,0:T(8,128)(2,1)S(1)}, bf16[256,256]{1,0:T(8,128)(2,1)S(1)}, u32[]{:S(2)}, u32[]{:S(2)}) collective-permute-start(bf16[256,256]{1,0:T(8,128)(2,1)S(1)} %get-tuple-element.125), channel_id=1, source_target_pairs={{0,2},{2,0},{4,6},{6,4},{8,10},{10,8},{12,14},{14,12},{16,18},{18,... | collective-permute-start | bytes 393224 | tf_op jit(solution)/shard_map/ppermute | solution.py:33
  126.2 9.5 %collective-permute-start.15 = (bf16[256,256]{1,0:T(8,128)(2,1)S(1)}, bf16[256,256]{1,0:T(8,128)(2,1)S(1)}, u32[]{:S(2)}, u32[]{:S(2)}) collective-permute-start(bf16[256,256]{1,0:T(8,128)(2,1)S(1)} %get-tuple-element.126), channel_id=1, source_target_pairs={{0,4},{2,6},{4,0},{6,2},{8,12},{10,14},{12,8},{14,10},{16,20},{18,... | collective-permute-start | bytes 393224 | tf_op jit(solution)/shard_map/ppermute | solution.py:33
  128.6 6.4 %copy-start.39 = (f32[256,1]{1,0:T(8,128)S(1)}, f32[256,1]{1,0:T(8,128)}, u32[]{:S(2)}) copy-start(f32[256,1]{1,0:T(8,128)} %get-tuple-element.75) | copy-start | bytes 3076
  133.5 8.3 %collective-permute-start.13 = (f32[8,1024]{1,0:T(8,128)}, f32[8,1024]{1,0:T(8,128)S(1)}, u32[]{:S(2)}, u32[]{:S(2)}) collective-permute-start(f32[8,1024]{1,0:T(8,128)} %get-tuple-element.91), channel_id=1, source_target_pairs={{2,0},{4,2},{6,4},{8,6},{10,8},{12,10},{14,12},{16,14},{18,16},{20... | collective-permute-start | bytes 98312 | tf_op jit(solution)/shard_map/ppermute | solution.py:28
  136.7 10.5 %copy-start.10 = (bf16[256,1024]{1,0:T(8,128)(2,1)S(1)}, bf16[256,1024]{1,0:T(8,128)(2,1)}, u32[]{:S(2)}) copy-start(bf16[256,1024]{1,0:T(8,128)(2,1)} %get-tuple-element.80.gate_grad_ref) | copy-start | bytes 1572868
  139.0 13.2 %collective-permute-start.20 = (bf16[128,1024]{1,0:T(8,128)(2,1)}, bf16[128,1024]{1,0:T(8,128)(2,1)S(1)}, u32[]{:S(2)}, u32[]{:S(2)}) collective-permute-start(bf16[128,1024]{1,0:T(8,128)(2,1)} %get-tuple-element.94.rest_0_), channel_id=1, source_target_pairs={{0,16},{2,6},{4,20},{6,2},{8,24},{10,14},{12,28},{14,10},{16,0},{1... | collective-permute-start | bytes 786440 | tf_op jit(solution)/shard_map/ppermute | solution.py:112
  143.9 25.9 %collective-permute-start.26 = (bf16[256,1024]{1,0:T(8,128)(2,1)}, bf16[256,1024]{1,0:T(8,128)(2,1)S(1)}, u32[]{:S(2)}, u32[]{:S(2)}) collective-permute-start(bf16[256,1024]{1,0:T(8,128)(2,1)} %patched.1.wait_ref.own_ref), channel_id=1, source_target_pairs={{0,4},{2,6},{4,0},{6,2},{8,12},{10,14},{12,8},{14,10},{16,20},{18,... | collective-permute-start | bytes 1572872 | tf_op jit(solution)/shard_map/ppermute | solution.py:33
  147.2 13.2 %collective-permute-start.22 = (bf16[64,1024]{1,0:T(8,128)(2,1)}, bf16[64,1024]{1,0:T(8,128)(2,1)S(1)}, u32[]{:S(2)}, u32[]{:S(2)}) collective-permute-start(bf16[64,1024]{1,0:T(8,128)(2,1)} %get-tuple-element.99.rest_1_), channel_id=1, source_target_pairs={{0,2},{2,0},{4,6},{6,4},{8,10},{10,8},{12,14},{14,12},{16,18},{18,... | collective-permute-start | bytes 393224 | tf_op jit(solution)/shard_map/ppermute | solution.py:33
  147.2 4.1 %copy-start.44 = (f32[1024]{0:T(1024)S(1)}, f32[1024]{0:T(1024)}, u32[]{:S(2)}) copy-start(f32[1024]{0:T(1024)} %param.14) | copy-start | bytes 12292
  151.2 19.4 %copy-start.3 = (f32[256,1024]{1,0:T(8,128)}, f32[256,1024]{1,0:T(8,128)S(1)}, u32[]{:S(2)}) copy-start(f32[256,1024]{1,0:T(8,128)S(1)} %fusion.10) | copy-start | bytes 3145732
  151.2 6.0 %copy-start.41 = (bf16[64,1024]{1,0:T(8,128)(2,1)S(1)}, bf16[64,1024]{1,0:T(8,128)(2,1)}, u32[]{:S(2)}) copy-start(bf16[64,1024]{1,0:T(8,128)(2,1)} %get-tuple-element.100.rest_2_) | copy-start | bytes 393220
  151.2 9.2 %copy-start.40 = (bf16[64,1024]{1,0:T(8,128)(2,1)S(1)}, bf16[64,1024]{1,0:T(8,128)(2,1)}, u32[]{:S(2)}) copy-start(bf16[64,1024]{1,0:T(8,128)(2,1)} %get-tuple-element.101.rest_3_) | copy-start | bytes 393220
  151.2 12.4 %copy-start.7 = (bf16[256,1024]{1,0:T(8,128)(2,1)S(1)}, bf16[256,1024]{1,0:T(8,128)(2,1)}, u32[]{:S(2)}) copy-start(bf16[256,1024]{1,0:T(8,128)(2,1)} %patched.1.wait_ref.own_ref) | copy-start | bytes 1572868
  152.3 17.5 %copy-start.50 = (f32[256]{0:T(256)}, f32[256]{0:T(256)S(1)}, u32[]{:S(2)}) copy-start(f32[256]{0:T(256)S(1)} %get-tuple-element.117) | copy-start | bytes 3076
  154.8 11.7 %collective-permute-start.21 = (bf16[128,1024]{1,0:T(8,128)(2,1)}, bf16[128,1024]{1,0:T(8,128)(2,1)S(1)}, u32[]{:S(2)}, u32[]{:S(2)}) collective-permute-start(bf16[128,1024]{1,0:T(8,128)(2,1)} %settled.1.held_ref), channel_id=1, source_target_pairs={{0,16},{2,6},{4,20},{6,2},{8,24},{10,14},{12,28},{14,10},{16,0},{1... | collective-permute-start | bytes 786440 | tf_op jit(solution)/shard_map/ppermute | solution.py:112
  156.5 3.8 %collective-permute-start.27 = (f32[1,1024]{1,0:T(1,128)}, f32[1,1024]{1,0:T(1,128)S(1)}, u32[]{:S(2)}, u32[]{:S(2)}) collective-permute-start(f32[1,1024]{1,0:T(1,128)} %bitcast.35), channel_id=1, source_target_pairs={{0,1},{1,0},{2,3},{3,2},{4,5},{5,4},{6,7},{7,6},{8,9},{9,8},{10,11... | collective-permute-start | bytes 12296 | tf_op jit(solution)/shard_map/ppermute | solution.py:33
  157.2 6.4 %collective-permute-start.23 = (bf16[64,1024]{1,0:T(8,128)(2,1)S(1)}, bf16[64,1024]{1,0:T(8,128)(2,1)S(1)}, u32[]{:S(2)}, u32[]{:S(2)}) collective-permute-start(bf16[64,1024]{1,0:T(8,128)(2,1)S(1)} %copy-done.41), channel_id=1, source_target_pairs={{0,4},{2,6},{4,0},{6,2},{8,12},{10,14},{12,8},{14,10},{16,20},{18,... | collective-permute-start | bytes 393224 | tf_op jit(solution)/shard_map/ppermute | solution.py:33
  160.4 6.2 %collective-permute-start.24 = (bf16[64,1024]{1,0:T(8,128)(2,1)S(1)}, bf16[64,1024]{1,0:T(8,128)(2,1)S(1)}, u32[]{:S(2)}, u32[]{:S(2)}) collective-permute-start(bf16[64,1024]{1,0:T(8,128)(2,1)S(1)} %copy-done.40), channel_id=1, source_target_pairs={{0,6},{2,4},{4,2},{6,0},{8,14},{10,12},{12,10},{14,8},{16,22},{18,... | collective-permute-start | bytes 393224 | tf_op jit(solution)/shard_map/ppermute | solution.py:33
  160.4 6.2 %copy-start.17 = (bf16[64,1024]{1,0:T(8,128)(2,1)}, bf16[64,1024]{1,0:T(8,128)(2,1)S(1)}, u32[]{:S(2)}) copy-start(bf16[64,1024]{1,0:T(8,128)(2,1)S(1)} %collective-permute-done.22.rest_0_.refs_4_.first_ref) | copy-start | bytes 393220
  160.4 9.4 %collective-permute-start.19 = (f32[1,256]{1,0:T(1,128)S(1)}, f32[1,256]{1,0:T(1,128)S(1)}, u32[]{:S(2)}, u32[]{:S(2)}) collective-permute-start(f32[1,256]{1,0:T(1,128)S(1)} %bitcast.44), channel_id=1, source_target_pairs={{0,1},{1,0},{2,3},{3,2},{4,5},{5,4},{6,7},{7,6},{8,9},{9,8},{10,11... | collective-permute-start | bytes 3080 | tf_op jit(solution)/shard_map/ppermute | solution.py:33
  163.6 9.2 %collective-permute-start.28 = (bf16[256,1024]{1,0:T(8,128)(2,1)S(1)}, bf16[256,1024]{1,0:T(8,128)(2,1)}, u32[]{:S(2)}, u32[]{:S(2)}) collective-permute-start(bf16[256,1024]{1,0:T(8,128)(2,1)S(1)} %copy-done.7), channel_id=1, source_target_pairs={{0,2},{2,0},{4,6},{6,4},{8,10},{10,8},{12,14},{14,12},{16,18},{18,... | collective-permute-start | bytes 1572872 | tf_op jit(solution)/shard_map/ppermute | solution.py:33
  170.6 10.2 %copy-start.6 = (bf16[256,1024]{1,0:T(8,128)(2,1)S(1)}, bf16[256,1024]{1,0:T(8,128)(2,1)}, u32[]{:S(2)}) copy-start(bf16[256,1024]{1,0:T(8,128)(2,1)} %unfolded.3.refs_1_.held_ref) | copy-start | bytes 1572868
  170.6 2.3 collective-permute-start.29
  171.5 14.5 %collective-permute-start.18 = (f32[256,512]{1,0:T(8,128)}, f32[256,512]{1,0:T(8,128)S(1)}, u32[]{:S(2)}, u32[]{:S(2)}) collective-permute-start(f32[256,512]{1,0:T(8,128)} %slice_select_fusion), channel_id=1, source_target_pairs={{0,1},{1,0},{2,3},{3,2},{4,5},{5,4},{6,7},{7,6},{8,9},{9,8},{10,11... | collective-permute-start | bytes 1572872 | tf_op jit(solution)/shard_map/ppermute | solution.py:33
  176.4 9.7 %collective-permute-start.30 = (bf16[80,1024]{1,0:T(8,128)(2,1)}, bf16[80,1024]{1,0:T(8,128)(2,1)S(1)}, u32[]{:S(2)}, u32[]{:S(2)}) collective-permute-start(bf16[80,1024]{1,0:T(8,128)(2,1)} %get-tuple-element.104), channel_id=1, source_target_pairs={{0,8},{2,10},{4,12},{6,14},{8,0},{10,2},{12,4},{14,6},{16,24},{18,... | collective-permute-start | bytes 491528 | tf_op jit(solution)/shard_map/ppermute | solution.py:33
  177.3 17.5 %collective-permute-start.31 = (bf16[80,1024]{1,0:T(8,128)(2,1)}, bf16[80,1024]{1,0:T(8,128)(2,1)S(1)}, u32[]{:S(2)}, u32[]{:S(2)}) collective-permute-start(bf16[80,1024]{1,0:T(8,128)(2,1)} %get-tuple-element.105), channel_id=1, source_target_pairs={{0,16},{2,18},{4,20},{6,22},{8,24},{10,26},{12,28},{14,30},{16,0},... | collective-permute-start | bytes 491528 | tf_op jit(solution)/shard_map/ppermute | solution.py:33
  178.1 16.6 %collective-permute-start.32 = (bf16[80,1024]{1,0:T(8,128)(2,1)}, bf16[80,1024]{1,0:T(8,128)(2,1)S(1)}, u32[]{:S(2)}, u32[]{:S(2)}) collective-permute-start(bf16[80,1024]{1,0:T(8,128)(2,1)} %get-tuple-element.106), channel_id=1, source_target_pairs={{0,24},{2,26},{4,28},{6,30},{8,16},{10,18},{12,20},{14,22},{16,8},... | collective-permute-start | bytes 491528 | tf_op jit(solution)/shard_map/ppermute | solution.py:33
  180.8 18.9 %collective-permute-start.25 = (bf16[256,1024]{1,0:T(8,128)(2,1)S(1)}, bf16[256,1024]{1,0:T(8,128)(2,1)S(1)}, u32[]{:S(2)}, u32[]{:S(2)}) collective-permute-start(bf16[256,1024]{1,0:T(8,128)(2,1)S(1)} %copy-done.6), channel_id=1, source_target_pairs={{0,8},{2,18},{4,12},{6,22},{8,0},{10,26},{12,4},{14,30},{16,24},{1... | collective-permute-start | bytes 1572872 | tf_op jit(solution)/shard_map/ppermute | solution.py:112
  202.7 24.3 %copy-start.24 = (bf16[80,1024]{1,0:T(8,128)(2,1)S(1)}, bf16[80,1024]{1,0:T(8,128)(2,1)}, u32[]{:S(2)}) copy-start(bf16[80,1024]{1,0:T(8,128)(2,1)} %pad_maximum_fusion.4.rest_0_) | copy-start | bytes 491524
  202.7 15.0 %collective-permute-start.33 = (bf16[512,1024]{1,0:T(8,128)(2,1)}, bf16[512,1024]{1,0:T(8,128)(2,1)S(1)}, u32[]{:S(2)}, u32[]{:S(2)}) collective-permute-start(bf16[512,1024]{1,0:T(8,128)(2,1)} %unfolded.4.held_ref), channel_id=1, source_target_pairs={{0,4},{2,10},{4,0},{6,14},{8,12},{10,2},{12,8},{14,6},{16,20},{18,... | collective-permute-start | bytes 3145736 | tf_op jit(solution)/shard_map/ppermute | solution.py:112
  221.7 27.2 %collective-permute-start.34 = (bf16[1024,1024]{1,0:T(8,128)(2,1)}, bf16[1024,1024]{1,0:T(8,128)(2,1)S(1)}, u32[]{:S(2)}, u32[]{:S(2)}) collective-permute-start(bf16[1024,1024]{1,0:T(8,128)(2,1)} %unfolded.5.refs_1_.own_ref.own_gate), channel_id=1, source_target_pairs={{0,2},{2,0},{4,6},{6,4},{8,10},{10,8},{12,14},{14,12},{16,18},{18,... | collective-permute-start | bytes 6291464 | tf_op jit(solution)/shard_map/ppermute | solution.py:33
  227.0 13.9 %collective-permute-start.36 = (bf16[80,1024]{1,0:T(8,128)(2,1)S(1)}, bf16[80,1024]{1,0:T(8,128)(2,1)S(1)}, u32[]{:S(2)}, u32[]{:S(2)}) collective-permute-start(bf16[80,1024]{1,0:T(8,128)(2,1)S(1)} %copy-done.24), channel_id=1, source_target_pairs={{0,16},{2,18},{4,20},{6,22},{8,24},{10,26},{12,28},{14,30},{16,0},... | collective-permute-start | bytes 491528 | tf_op jit(solution)/shard_map/ppermute | solution.py:33
  228.0 12.9 %collective-permute-start.35 = (bf16[80,1024]{1,0:T(8,128)(2,1)S(1)}, bf16[80,1024]{1,0:T(8,128)(2,1)S(1)}, u32[]{:S(2)}, u32[]{:S(2)}) collective-permute-start(bf16[80,1024]{1,0:T(8,128)(2,1)S(1)} %copy-done.24), channel_id=1, source_target_pairs={{0,24},{2,26},{4,28},{6,30},{8,16},{10,18},{12,20},{14,22},{16,8},... | collective-permute-start | bytes 491528 | tf_op jit(solution)/shard_map/ppermute | solution.py:33
  229.6 12.5 %collective-permute-start.37 = (bf16[80,1024]{1,0:T(8,128)(2,1)S(1)}, bf16[80,1024]{1,0:T(8,128)(2,1)S(1)}, u32[]{:S(2)}, u32[]{:S(2)}) collective-permute-start(bf16[80,1024]{1,0:T(8,128)(2,1)S(1)} %copy-done.24), channel_id=1, source_target_pairs={{0,8},{2,10},{4,12},{6,14},{8,0},{10,2},{12,4},{14,6},{16,24},{18,... | collective-permute-start | bytes 491528 | tf_op jit(solution)/shard_map/ppermute | solution.py:33
  242.8 5.0 %copy-start.49 = (f32[1,256]{1,0:T(1,128)S(1)}, f32[1,256]{1,0:T(1,128)}, u32[]{:S(2)}) copy-start(f32[1,256]{1,0:T(1,128)} %copy-done.48) | copy-start | bytes 3076
  242.8 5.0 %copy-start.51 = (f32[256]{0:T(256)S(1)}, f32[256]{0:T(256)}, u32[]{:S(2)}) copy-start(f32[256]{0:T(256)} %copy-done.50) | copy-start | bytes 3076
  242.8 5.0 %copy-start.4 = (f32[256,1024]{1,0:T(8,128)S(1)}, f32[256,1024]{1,0:T(8,128)}, u32[]{:S(2)}) copy-start(f32[256,1024]{1,0:T(8,128)} %copy-done.3) | copy-start | bytes 3145732
  242.8 5.0 %copy-start.9 = (bf16[256,512]{1,0:T(8,128)(2,1)S(1)}, bf16[256,512]{1,0:T(8,128)(2,1)}, u32[]{:S(2)}) copy-start(bf16[256,512]{1,0:T(8,128)(2,1)} %own_ref.1) | copy-start | bytes 786436
  242.8 5.0 %copy-start.13 = (f32[256,512]{1,0:T(8,128)S(1)}, f32[256,512]{1,0:T(8,128)}, u32[]{:S(2)}) copy-start(f32[256,512]{1,0:T(8,128)} %copy-done.12) | copy-start | bytes 1572868
  242.8 5.0 %copy-start.15 = (f32[256,512]{1,0:T(8,128)S(1)}, f32[256,512]{1,0:T(8,128)}, u32[]{:S(2)}) copy-start(f32[256,512]{1,0:T(8,128)} %copy-done.14) | copy-start | bytes 1572868
  242.8 5.0 %copy-start.23 = (bf16[256,512]{1,0:T(8,128)(2,1)S(1)}, bf16[256,512]{1,0:T(8,128)(2,1)}, u32[]{:S(2)}) copy-start(bf16[256,512]{1,0:T(8,128)(2,1)} %param.25) | copy-start | bytes 786436
  242.8 5.0 %copy-start.52 = (f32[256]{0:T(256)S(1)}, f32[256]{0:T(256)}, u32[]{:S(2)}) copy-start(f32[256]{0:T(256)} %get-tuple-element.119) | copy-start | bytes 3076
  246.0 2.8 %collective-permute-start.39 = (bf16[320,1024]{1,0:T(8,128)(2,1)}, bf16[320,1024]{1,0:T(8,128)(2,1)}, u32[]{:S(2)}, u32[]{:S(2)}) collective-permute-start(bf16[320,1024]{1,0:T(8,128)(2,1)} %pad_maximum_fusion.first_ref.rest_0_), channel_id=1, source_target_pairs={{0,2},{2,0},{4,6},{6,4},{8,10},{10,8},{12,14},{14,12},{16,18},{18,... | collective-permute-start | bytes 1966088 | tf_op jit(solution)/shard_map/ppermute | solution.py:33
  246.0 17.5 %collective-permute-start.38 = (bf16[320,1024]{1,0:T(8,128)(2,1)}, bf16[320,1024]{1,0:T(8,128)(2,1)}, u32[]{:S(2)}, u32[]{:S(2)}) collective-permute-start(bf16[320,1024]{1,0:T(8,128)(2,1)} %pad_maximum_fusion.first_ref.rest_0_), channel_id=1, source_target_pairs={{0,4},{2,6},{4,0},{6,2},{8,12},{10,14},{12,8},{14,10},{16,20},{18,... | collective-permute-start | bytes 1966088 | tf_op jit(solution)/shard_map/ppermute | solution.py:33
  263.5 2.3 collective-permute-start.40
  266.6 6.4 %copy-start.1 = (bf16[1024,1024]{1,0:T(8,128)(2,1)S(1)}, bf16[1024,1024]{1,0:T(8,128)(2,1)}, u32[]{:S(2)}) copy-start(bf16[1024,1024]{1,0:T(8,128)(2,1)} %param.23) | copy-start | bytes 6291460
  (30 other events, 29.2 us)

commit v14 on v13

--- a/solution.py
+++ b/solution.py
@@ -923,7 +923,6 @@
     own_ref,
     near_ref,
     far_ref,
-    last_ref,
     normed_0,
     normed_1,
     normed_2,
@@ -936,9 +935,10 @@
 ):
     keep_ref, *sends_refs, piece, small = rest[-6:]
     total = None
-    grads = (own_ref, near_ref, far_ref, last_ref)
+    tokens = own_ref.shape[0]
+    grads = (own_ref[...], near_ref[...], far_ref[:tokens, :], far_ref[tokens:, :])
     for left, right in zip((normed_0, normed_1, normed_2, normed_3), grads):
-        part = lax.dot_general(left[...], right[...], contract_first, preferred_element_type=f32)
+        part = lax.dot_general(left[...], right, contract_first, preferred_element_type=f32)
         total = part if total is None else total + part
     piece[...] = total
     small[...] = small_ref[...] + sum(
@@ -957,7 +957,7 @@
             sends_refs[n - 1][rows:, :] = small_rows.astype(bf16)
 
 
-def inner_quarter(place, own, near, far, last, normed, smalls, waits):
+def inner_quarter(place, own, near, far, normed, smalls, waits):
     width = own.shape[1]
     quarter = normed[0].shape[1]
     spare = smalls[0].shape[0]
@@ -965,7 +965,7 @@
     return pl.pallas_call(
         quarter_kernel,
         in_specs=[pl.BlockSpec(memory_space=pltpu.SMEM)]
-        + [pl.BlockSpec(memory_space=pltpu.VMEM)] * 12
+        + [pl.BlockSpec(memory_space=pltpu.VMEM)] * 11
         + [pl.BlockSpec(memory_space=pl.ANY)] * len(waits),
         out_shape=[jax.ShapeDtypeStruct((rows, width), f32)]
         + [jax.ShapeDtypeStruct((rows, width), bf16)] * 3,
@@ -973,7 +973,7 @@
         compiler_params=pltpu.CompilerParams(vmem_limit_bytes=vmem_bytes),
         cost_estimate=tiny_cost,
         name="inner_quarter",
-    )(place, own, near, far, last, *normed, *smalls, *waits)
+    )(place, own, near, far, *normed, *smalls, *waits)
 
 
 def join_kernel(place_ref, own_gate, other_gate, first_ref, second_ref, *rest, small_rows):
@@ -1382,8 +1382,8 @@
         arrived = early_swapped(send, bits)
     inner_grad = patched(segment_ids, inner_main, last, following, send)
     near = swapped(inner_grad, "wide", 2)
-    far = swapped(inner_grad, "wide", 1)
-    keep, *sends = small_quarters(four_place, scan_smalls, conv_small, inner_grad)
+    early = settled(early, arrived, inner_grad)
+    keep, *sends = small_quarters(four_place, scan_smalls, conv_small, early)
     smalls = [keep] + [swapped(sends[n - 1], "wide", n) for n in (1, 2, 3)]
     normed_part = jnp.einsum(
         "cte,dce->td", jnp.stack([inner_grad, gate_grad]), in_weight, preferred_element_type=f32
@@ -1393,26 +1393,23 @@
     gain_sum = gain_part + swapped(gain_part, "narrow", 1)
     for bit in (bit for bits in more_bits for bit in bits):
         gain_sum = gain_sum + swapped(gain_sum, "wide", bit)
-    early = settled(early, arrived, gain_part, *sends)
-    for bits in steps[:1:-1]:
-        back = early_swapped(early, bits)
-        early = unfolded(early, back, bits, *smalls[1:])
-    back = early_swapped(early, steps[1])
+    near = after(near, gain_part, *smalls[1:])
+    far = swapped(jnp.concatenate([inner_grad, near]), "wide", 1)
     normed_mine, normed_other = narrow_halves(normed_part)
     row_theirs = swapped(row_part, "narrow", 1)
     normed_theirs = swapped(normed_other, "narrow", 1)
-    near = after(near, early, gain_sum, row_theirs, *smalls[1:])
-    last = swapped(near, "wide", 1)
     keep, *sends = inner_quarter(
         (wide_place >> 2 & 3)[None],
         inner_grad,
         near,
         far,
-        last,
         normed_four,
         smalls,
-        [],
-    )
+        [gain_sum, row_theirs],
+    )
+    for bits in steps[:1:-1]:
+        early = unfolded(early, early_swapped(early, bits), bits, keep)
+    back = early_swapped(early, steps[1])
     row_sum = (row_part + row_theirs).reshape(rows, 1)
     gain_mine = jnp.where(right_half, norm_gain[features:], norm_gain[:features])
     whole_grad = inverse * (gain_mine * (normed_mine + normed_theirs)) - tokens.astype(f32) * (
@@ -1420,7 +1417,7 @@
     ) * (row_sum / (2 * features))
     tokens_grad = (whole_grad + cotangent.astype(f32)).astype(bf16)
     arrived = [swapped(sends[n - 1], "wide", flips(first_bits)[n]) for n in (1, 2, 3)]
-    arrived[0] = after(arrived[0], normed_theirs)
+    arrived[0] = after(arrived[0], normed_theirs, early)
     held = keep + sum(a.astype(f32) for a in arrived)
     for bits in more_bits:
         held = scattered(held, bits)
@@ -1430,10 +1427,11 @@
     spare = jnp.broadcast_to(gain_sum, (block_rows - used_rows, gain_sum.shape[1]))
     held = jnp.concatenate([held[: held.shape[0] - spare.shape[0]], spare.astype(bf16)])
     early = unfolded(early, back, steps[1], held)
-    early = unfolded(early, early_swapped(early, steps[0]), steps[0])
+    back = early_swapped(early, steps[0])
     held = gathered(held, first_bits, early)
+    core = swapped(held, "wide", 1)
+    early = unfolded(early, back, steps[0], core)
     core_early = swapped(early, "wide", 1)
-    core = swapped(held, "wide", 1)
     out_weight_grad = widened(four_place, early, core_early, core)
     gates = (early, core_early)
     (begun,) = joined(

time: 275 us -> 277 us (level)
  starting transfers between devices: 54 us -> 62.4 us
  waiting for transfers between devices: 63.1 us -> 58.9 us
    ppermute x6, waiting for transfers between devices: 16.4 us -> 5.29 us  [early_swapped(): lax.ppermute(array, 'wide', [(i, i ^ bits[i % 2]) for i in range(peers)])]
    ppermute x30 -> x29, starting transfers between devices: 31.8 us -> 41.4 us  [swapped(): return lax.ppermute(array, axis, [(i, i ^ bit) for i in range(peers)])]
    ppermute x30 -> x29, waiting for transfers between devices: 46.7 us -> 53.5 us  [swapped(): return lax.ppermute(array, axis, [(i, i ^ bit) for i in range(peers)])]
    unnamed x106 -> x96, local copies, waits for them, and re-layouts: 15.4 us -> 13.6 us
  transfers between devices with their start and end apart: 41 -> 40, of which waited for: 16 -> 17; matrix products, arithmetic and copies ran while one was open for 10% -> 9% of each run, Pallas kernels for 28% -> 29%
where the time goes in v14:
time: 277 us; the launch traced here: 275 us
  Pallas kernels  111 us (40%)
  starting transfers between devices  62.4 us (23%)
  waiting for transfers between devices  58.9 us (21%)
  local copies, waits for them, and re-layouts  16.9 us (6%)
  matrix products  12.4 us (4%)
  other arithmetic  12.3 us (4%)
    pallas_call x6, Pallas kernels, call(): pl.pallas_call(kernel, grid=(width // scan_width,), in_specs=in_specs, ou...  57.3 us
    ppermute x29, waiting for transfers between devices, swapped(): return lax.ppermute(array, axis, [(i, i ^ bit) for i in range(peers)])  53.5 us
    ppermute x29, starting transfers between devices, swapped(): return lax.ppermute(array, axis, [(i, i ^ bit) for i in range(peers)])  41.4 us
    pallas_call x8, Pallas kernels, small_call(): pl.pallas_call(functools.partial(kernel, waits=len(waits)), in_specs=[pl....  23.2 us
    unnamed x96, local copies, waits for them, and re-layouts  13.6 us
    ppermute x4, starting transfers between devices, passed_along(): return lax.ppermute(array, axis, pairs)  11.5 us
    pallas_call x2, Pallas kernels, joined(): pl.pallas_call(functools.partial(join_kernel, small_rows=small_rows), gri...  11.2 us
    ppermute x6, starting transfers between devices, early_swapped(): lax.ppermute(array, 'wide', [(i, i ^ bits[i % 2]) for i in range(peers)])  8.1 us
  transfers between devices with their start and end apart: 40, of which 17 were waited for; matrix products, arithmetic and copies ran while one was open for 9% of the time, Pallas kernels for 29%

profile of v14, /device:TPU:0, one launch (start us, length us, event | category | flops | bytes accessed | tf_op | source)
XLA Modules:
  0.0 275.4 jit_solution(17997772166070710464)
XLA Ops:
  0.7 3.0 %collective-permute-start = (bf16[256,512]{1,0:T(8,128)(2,1)}, bf16[256,512]{1,0:T(8,128)(2,1)S(1)}, u32[]{:S(2)}, u32[]{:S(2)}) collective-permute-start(bf16[256,512]{1,0:T(8,128)(2,1)} %own_ref.1), channel_id=1, source_target_pairs={{0,1},{1,0},{2,3},{3,2},{4,5},{5,4},{6,7},{7,6},{8,9},{9,8},{10,11... | collective-permute-start | bytes 786440 | tf_op jit(solution)/shard_map/ppermute | solution.py:33
  3.7 1.4 edge_rows.1
  5.1 1.4 collective-permute-start.2
  6.5 4.0 %collective-permute-start.1 = (bf16[16,512]{1,0:T(8,128)(2,1)}, bf16[16,512]{1,0:T(8,128)(2,1)S(1)}, u32[]{:S(2)}, u32[]{:S(2)}) collective-permute-start(bf16[16,512]{1,0:T(8,128)(2,1)} %edge_rows.1), channel_id=1, source_target_pairs={{0,2},{2,4},{4,6},{6,8},{8,10},{10,12},{12,14},{14,16},{16,18},{18... | collective-permute-start | bytes 49160 | tf_op jit(solution)/shard_map/ppermute | solution.py:28
  10.5 1.5 collective-permute-start.4
  12.8 2.5 normalized.1
  15.3 4.9 %fusion.7.inner_ref.gate_ref = bf16[2,272,1024]{2,1,0:T(8,128)(2,1)} fusion(bf16[1024,2,1024]{2,1,0:T(2,128)(2,1)} %param.15, bf16[272,1024]{1,0:T(8,128)(2,1)} %get-tuple-element.64), kind=kOutput, calls=%fused_computation.5 | convolution fusion | flops 1141407744 | bytes 5865472 | tf_op jit(solution)/shard_map/td,dce->cte/dot_general | solution.py:1267
  20.2 3.5 %convolve.1 = (f32[256,1024]{1,0:T(8,128)}, bf16[256,1024]{1,0:T(8,128)(2,1)}, f32[96,256]{1,0:T(8,128)}) custom-call(bf16[2,272,1024]{2,1,0:T(8,128)(2,1)} %fusion.7.inner_ref.gate_ref, f32[4,1024]{1,0:T(4,128)} %conv_weight_ref.3, f32[1,1024]{1,0:T(1,128)} %bitcast.42, bf16[96,1024]{1,0:T(8,128)(2,1)} %select_ref.3, f32[256,128]{1,0:T(8,128)} %get-tuple-element.65.mask_ref), custom_call_target="tpu_custom_call" | custom-call | flops 1 | bytes 1 | tf_op jit(solution)/shard_map/convolve/pallas_call | solution.py:147
  24.8 1.8 fusion.28.gated_grad_ref
  26.6 2.1 collective-permute-done.3.other_ref
  29.3 10.7 %scan_ends.1 = (f32[256,1024]{1,0:T(8,128)}, f32[256,1024]{1,0:T(8,128)}, f32[40,1024]{1,0:T(8,128)}) custom-call(f32[96,256]{1,0:T(8,128)} %get-tuple-element.66.selected_ref, f32[96,256]{1,0:T(8,128)} %copy-done.17, bf16[64,1024]{1,0:T(8,128)(2,1)} %step_weight_ref.5, f32[1,1024]{1,0:T(1,128)} %bitcast.43, bf16[256,1024]{1,0:T(8,128)(2,1)} %get-tuple-element.67.act_ref, ...), custom_call_target="tpu_custom_call" | custom-call | flops 1 | bytes 1 | tf_op jit(solution)/shard_map/scan_ends/pallas_call | solution.py:147
  40.1 1.6 collective-permute-done.5.other_ref
  42.4 1.9 carry_round.2
  44.3 1.7 collective-permute-start.6
  46.0 4.8 %collective-permute-done.6.other_ref = f32[40,1024]{1,0:T(8,128)S(1)} collective-permute-done((f32[40,1024]{1,0:T(8,128)}, f32[40,1024]{1,0:T(8,128)S(1)}, u32[]{:S(2)}, u32[]{:S(2)}) %collective-permute-start.6) | collective-permute-done | bytes 163872 | tf_op jit(solution)/shard_map/ppermute | solution.py:33
  51.4 1.9 carry_round.3
  53.3 4.6 %collective-permute-start.7 = (f32[16,1024]{1,0:T(8,128)}, f32[16,1024]{1,0:T(8,128)S(1)}, u32[]{:S(2)}, u32[]{:S(2)}) collective-permute-start(f32[16,1024]{1,0:T(8,128)} %get-tuple-element.73), channel_id=1, source_target_pairs={{0,8},{2,10},{4,12},{6,14},{8,16},{10,18},{12,20},{14,22},{16,24},... | collective-permute-start | bytes 196616 | tf_op jit(solution)/shard_map/ppermute | solution.py:28
  60.7 10.4 %scan_forward.1 = (bf16[256,1024]{1,0:T(8,128)(2,1)}, bf16[256,1024]{1,0:T(8,128)(2,1)}, f32[16,1024]{1,0:T(8,128)}) custom-call(f32[96,256]{1,0:T(8,128)} %get-tuple-element.66.selected_ref, f32[96,256]{1,0:T(8,128)} %copy-done.17, f32[256,1024]{1,0:T(8,128)} %get-tuple-element.68.step_ref, bf16[256,1024]{1,0:T(8,128)(2,1)} %get-tuple-element.67.act_ref, ...), custom_call_target="tpu_custom_call" | custom-call | flops 1 | bytes 1 | tf_op jit(solution)/shard_map/scan_forward/pallas_call | solution.py:147
  71.7 3.6 %early_send.1 = bf16[1024,1024]{1,0:T(8,128)(2,1)} custom-call(s32[1]{0:T(128)} %bitcast.9.core_ref, bf16[256,1024]{1,0:T(8,128)(2,1)} %get-tuple-element.74.gated_ref, bf16[256,1024]{1,0:T(8,128)(2,1)} %pad_maximum_fusion.2.cot_ref, bf16[256,1024]{1,0:T(8,128)(2,1)} %get-tuple-element.79.normed_ref.refs_0_, ...), custom_call_target="tpu_custom_call" | custom-call | flops 1 | bytes 1 | tf_op jit(solution)/shard_map/early_send/pallas_call | solution.py:1058
  75.3 1.7 fusion.30
  77.9 1.9 collective-permute-done.10.arrived_ref
  79.8 5.2 %early_first.1 = (f32[512,1024]{1,0:T(8,128)}, bf16[512,1024]{1,0:T(8,128)(2,1)}) custom-call(s32[1]{0:T(128)} %bitcast.9.core_ref, s32[1]{0:T(128)} %bitcast.10.upper_ref, bf16[256,1024]{1,0:T(8,128)(2,1)} %get-tuple-element.74.gated_ref, bf16[256,1024]{1,0:T(8,128)(2,1)} %pad_maximum_fusion.2.cot_ref, ...), custom_call_target="tpu_custom_call" | custom-call | flops 1 | bytes 1 | tf_op jit(solution)/shard_map/early_first/pallas_call | solution.py:1058
  85.6 1.5 collective-permute-start.8
  87.7 13.9 %scan_backward.2 = (f32[256,512]{1,0:T(8,128)}, f32[96,256]{1,0:T(8,128)}, f32[82,512]{1,0:T(8,128)}) custom-call(f32[96,256]{1,0:T(8,128)} %get-tuple-element.66.selected_ref, f32[96,256]{1,0:T(8,128)} %copy-done.17, f32[256,1024]{1,0:T(8,128)} %get-tuple-element.76.step_pre_ref, f32[256,1024]{1,0:T(8,128)} %get-tuple-element.68.step_ref, ...), custom_call_target="tpu_custom_call" | custom-call | flops 1 | bytes 1 | tf_op jit(solution)/shard_map/scan_backward/pallas_call | solution.py:147
  102.6 3.2 %folded.2 = (f32[256,1024]{1,0:T(8,128)}, bf16[256,1024]{1,0:T(8,128)(2,1)}) custom-call(s32[1]{0:T(128)} %bitcast.11.upper_ref, f32[512,1024]{1,0:T(8,128)} %get-tuple-element.83.keep_ref, bf16[512,1024]{1,0:T(8,128)(2,1)} %copy-done.20, f32[96,256]{1,0:T(8,128)} %get-tuple-element.82.rest_0_.earlier_ref), custom_call_target="tpu_custom_call" | custom-call | flops 1 | bytes 1 | tf_op jit(solution)/shard_map/folded/pallas_call | solution.py:1058
  105.8 2.6 collective-permute-start.14
  108.4 13.9 %scan_backward.3 = (f32[256,512]{1,0:T(8,128)}, f32[96,256]{1,0:T(8,128)}, f32[82,512]{1,0:T(8,128)}) custom-call(f32[96,256]{1,0:T(8,128)} %get-tuple-element.66.selected_ref, f32[96,256]{1,0:T(8,128)} %copy-done.17, f32[256,1024]{1,0:T(8,128)} %get-tuple-element.76.step_pre_ref, f32[256,1024]{1,0:T(8,128)} %get-tuple-element.68.step_ref, ...), custom_call_target="tpu_custom_call" | custom-call | flops 1 | bytes 1 | tf_op jit(solution)/shard_map/scan_backward/pallas_call | solution.py:147
  122.9 1.9 constant_dynamic-slice_fusion
  128.6 4.9 %convolve_grad.1 = (bf16[256,1024]{1,0:T(8,128)(2,1)}, f32[8,1024]{1,0:T(8,128)}, f32[8,1024]{1,0:T(8,128)}, f32[101,1024]{1,0:T(8,128)}) custom-call(f32[96,256]{1,0:T(8,128)} %get-tuple-element.85.select_grad_ref.refs_1_, f32[96,256]{1,0:T(8,128)} %copy-done.39, bf16[96,1024]{1,0:T(8,128)(2,1)} %select_ref.3, f32[256,512]{1,0:T(8,128)} %get-tuple-element.86.first_act_grad, ...), custom_call_target="tpu_custom_call" | custom-call | flops 1 | bytes 1 | tf_op jit(solution)/shard_map/convolve_grad/pallas_call | solution.py:147
  133.4 1.6 collective-permute-start.13
  136.0 2.3 folded.3
  138.3 2.8 %collective-permute-start.20 = (bf16[128,1024]{1,0:T(8,128)(2,1)}, bf16[128,1024]{1,0:T(8,128)(2,1)}, u32[]{:S(2)}, u32[]{:S(2)}) collective-permute-start(bf16[128,1024]{1,0:T(8,128)(2,1)} %get-tuple-element.94.rest_0_), channel_id=1, source_target_pairs={{0,16},{2,6},{4,20},{6,2},{8,24},{10,14},{12,28},{14,10},{16,0},{1... | collective-permute-start | bytes 786440 | tf_op jit(solution)/shard_map/ppermute | solution.py:112
  141.7 1.4 patched.1.rest_0_.own_ref
  144.3 3.9 %fusion.10 = f32[256,1024]{1,0:T(8,128)S(1)} fusion(bf16[1024,2,1024]{2,1,0:T(2,128)(2,1)} %param.15, bf16[1,256,1024]{2,1,0:T(8,128)(2,1)S(1)} %bitcast.33, bf16[1,256,1024]{2,1,0:T(8,128)(2,1)} %bitcast.32), kind=kOutput, calls=%fused_computation.6 | convolution fusion | flops 1074266112 | bytes 6291456 | tf_op jit(solution)/shard_map/cte,dce->td/dot_general | solution.py:1388
  148.7 1.9 settled.1.wait_ref.held_ref
  150.6 2.3 small_quarters.1
  152.8 2.1 collective-permute-start.24
  155.1 1.9 fusion.15
  157.0 2.5 collective-permute-done.24.refs_3_.second_ref
  159.5 2.5 collective-permute-done.25.refs_4_.third_ref
  162.9 2.1 pad_maximum_fusion
  169.2 2.1 collective-permute-start.21
  171.3 9.2 %collective-permute-done.27 = f32[1,1024]{1,0:T(1,128)S(1)} collective-permute-done((f32[1,1024]{1,0:T(1,128)S(1)}, f32[1,1024]{1,0:T(1,128)S(1)}, u32[]{:S(2)}, u32[]{:S(2)}) %collective-permute-start.27) | collective-permute-done | bytes 4128 | tf_op jit(solution)/shard_map/ppermute | solution.py:33
  181.7 3.5 %inner_quarter.1 = (f32[80,1024]{1,0:T(8,128)}, bf16[80,1024]{1,0:T(8,128)(2,1)}, bf16[80,1024]{1,0:T(8,128)(2,1)}, bf16[80,1024]{1,0:T(8,128)(2,1)}) custom-call(s32[1]{0:T(128)} %bitcast.19.place_ref, bf16[256,1024]{1,0:T(8,128)(2,1)} %patched.1.rest_0_.own_ref, bf16[256,1024]{1,0:T(8,128)(2,1)} %after.6.near_ref, ...), custom_call_target="tpu_custom_call" | custom-call | flops 1 | bytes 1 | tf_op jit(solution)/shard_map/inner_quarter/pallas_call | solution.py:965
  185.4 3.4 %collective-permute-start.30 = (bf16[80,1024]{1,0:T(8,128)(2,1)}, bf16[80,1024]{1,0:T(8,128)(2,1)S(1)}, u32[]{:S(2)}, u32[]{:S(2)}) collective-permute-start(bf16[80,1024]{1,0:T(8,128)(2,1)} %get-tuple-element.105), channel_id=1, source_target_pairs={{0,16},{2,18},{4,20},{6,22},{8,24},{10,26},{12,28},{14,30},{16,0},... | collective-permute-start | bytes 491528 | tf_op jit(solution)/shard_map/ppermute | solution.py:33
  190.3 1.9 unfolded.3.refs_2_.held_ref
  192.2 1.5 collective-permute-done.29.refs_0_
  194.3 10.0 %collective-permute-done.30 = bf16[80,1024]{1,0:T(8,128)(2,1)S(1)} collective-permute-done((bf16[80,1024]{1,0:T(8,128)(2,1)}, bf16[80,1024]{1,0:T(8,128)(2,1)S(1)}, u32[]{:S(2)}, u32[]{:S(2)}) %collective-permute-start.30) | collective-permute-done | bytes 163872 | tf_op jit(solution)/shard_map/ppermute | solution.py:33
  205.5 7.6 %collective-permute-start.34 = (bf16[80,1024]{1,0:T(8,128)(2,1)S(1)}, bf16[80,1024]{1,0:T(8,128)(2,1)S(1)}, u32[]{:S(2)}, u32[]{:S(2)}) collective-permute-start(bf16[80,1024]{1,0:T(8,128)(2,1)S(1)} %pad_maximum_fusion.5.rest_0_), channel_id=1, source_target_pairs={{0,16},{2,18},{4,20},{6,22},{8,24},{10,26},{12,28},{14,30},{16,0},... | collective-permute-start | bytes 491528 | tf_op jit(solution)/shard_map/ppermute | solution.py:33
  213.1 1.5 collective-permute-start.33
  214.6 8.7 %collective-permute-done.34 = bf16[80,1024]{1,0:T(8,128)(2,1)S(1)} collective-permute-done((bf16[80,1024]{1,0:T(8,128)(2,1)S(1)}, bf16[80,1024]{1,0:T(8,128)(2,1)S(1)}, u32[]{:S(2)}, u32[]{:S(2)}) %collective-permute-start.34) | collective-permute-done | bytes 163872 | tf_op jit(solution)/shard_map/ppermute | solution.py:33
  224.7 2.2 unfolded.4.refs_1_.held_ref
  229.7 5.5 %collective-permute-start.36 = (bf16[320,1024]{1,0:T(8,128)(2,1)}, bf16[320,1024]{1,0:T(8,128)(2,1)S(1)}, u32[]{:S(2)}, u32[]{:S(2)}) collective-permute-start(bf16[320,1024]{1,0:T(8,128)(2,1)} %pad_maximum_fusion.1.first_ref.rest_0_), channel_id=1, source_target_pairs={{0,2},{2,0},{4,6},{6,4},{8,10},{10,8},{12,14},{14,12},{16,18},{18,... | collective-permute-start | bytes 1966088 | tf_op jit(solution)/shard_map/ppermute | solution.py:33
  235.2 1.9 collective-permute-done.36.rest_0_.wait_ref.second_ref.rest_1_
  237.2 4.8 %collective-permute-done.32.arrived_ref = bf16[512,1024]{1,0:T(8,128)(2,1)S(1)} collective-permute-done((bf16[512,1024]{1,0:T(8,128)(2,1)}, bf16[512,1024]{1,0:T(8,128)(2,1)S(1)}, u32[]{:S(2)}, u32[]{:S(2)}) %collective-permute-start.32) | collective-permute-done | bytes 1048608 | tf_op jit(solution)/shard_map/ppermute | solution.py:112
  242.9 3.0 %unfolded.5.own_ref.own_gate = bf16[1024,1024]{1,0:T(8,128)(2,1)} custom-call(s32[1]{0:T(128)} %bitcast.10.upper_ref, bf16[512,1024]{1,0:T(8,128)(2,1)} %unfolded.4.refs_1_.held_ref, bf16[512,1024]{1,0:T(8,128)(2,1)} %copy-done.19, bf16[320,1024]{1,0:T(8,128)(2,1)} %copy-done.3), custom_call_target="tpu_custom_call" | custom-call | flops 1 | bytes 1 | tf_op jit(solution)/shard_map/unfolded/pallas_call | solution.py:1058
  245.9 2.8 %collective-permute-start.37 = (bf16[1024,1024]{1,0:T(8,128)(2,1)}, bf16[1024,1024]{1,0:T(8,128)(2,1)S(1)}, u32[]{:S(2)}, u32[]{:S(2)}) collective-permute-start(bf16[1024,1024]{1,0:T(8,128)(2,1)} %unfolded.5.own_ref.own_gate), channel_id=1, source_target_pairs={{0,2},{2,0},{4,6},{6,4},{8,10},{10,8},{12,14},{14,12},{16,18},{18,... | collective-permute-start | bytes 6291464 | tf_op jit(solution)/shard_map/ppermute | solution.py:33
  250.8 2.0 collective-permute-done.37.other_ref.other_gate
  252.7 1.3 copy-done.2
  254.1 4.7 %widened.1.rest_2_ = f32[1024,1024]{1,0:T(8,128)} custom-call(s32[1]{0:T(128)} %bitcast.18.place_ref, bf16[1024,1024]{1,0:T(8,128)(2,1)} %unfolded.5.own_ref.own_gate, bf16[1024,1024]{1,0:T(8,128)(2,1)} %copy-done.2, bf16[320,1024]{1,0:T(8,128)(2,1)} %copy-done.3), custom_call_target="tpu_custom_call" | custom-call | flops 1 | bytes 1 | tf_op jit(solution)/shard_map/widened/pallas_call | solution.py:1166
  258.8 4.8 %joined.2.refs_1_.rest_4_ = f32[1024,2,1024]{2,1,0:T(2,128)} custom-call(s32[1]{0:T(128)} %bitcast.18.place_ref, bf16[1024,1024]{1,0:T(8,128)(2,1)} %unfolded.5.own_ref.own_gate, bf16[1024,1024]{1,0:T(8,128)(2,1)} %copy-done.2, bf16[320,1024]{1,0:T(8,128)(2,1)} %pad_maximum_fusion.1.first_ref.rest_0_, bf16[320,1024]{1,0:T(8,128)(2,1)} %copy-done.3, ...), custom_call_target="tpu_custom_call" | custom-call | flops 1 | bytes 1 | tf_op jit(solution)/shard_map/joined/pallas_call | solution.py:1031
  263.6 2.1 collective-permute-done.38.refs_0_
  265.7 2.3 collective-permute-done.39.second_ref.rest_3_
  268.8 6.4 %joined.3 = (f32[1024,2,1024]{2,1,0:T(2,128)}, f32[64,1024]{1,0:T(8,128)}, f32[16,1024]{1,0:T(8,128)}, f32[1,1024]{1,0:T(1,128)}, f32[1,1024]{1,0:T(1,128)}, /*i...) custom-call(s32[1]{0:T(128)} %bitcast.18.place_ref, ...), custom_call_target="tpu_custom_call", output_to_operand_aliasing={{0}: (9, {})} | custom-call | flops 1 | bytes 1 | tf_op jit(solution)/shard_map/joined/pallas_call | solution.py:1031
  (166 shorter events, 35.7 us)
Async XLA Ops:
  0.6 24.2 %copy-start = (bf16[1024,1024]{1,0:T(8,128)(2,1)S(1)}, bf16[1024,1024]{1,0:T(8,128)(2,1)}, u32[]{:S(2)}) copy-start(bf16[1024,1024]{1,0:T(8,128)(2,1)} %param.23) | copy-start | bytes 6291460
  0.7 11.4 %collective-permute-start = (bf16[256,512]{1,0:T(8,128)(2,1)}, bf16[256,512]{1,0:T(8,128)(2,1)S(1)}, u32[]{:S(2)}, u32[]{:S(2)}) collective-permute-start(bf16[256,512]{1,0:T(8,128)(2,1)} %own_ref.1), channel_id=1, source_target_pairs={{0,1},{1,0},{2,3},{3,2},{4,5},{5,4},{6,7},{7,6},{8,9},{9,8},{10,11... | collective-permute-start | bytes 786440 | tf_op jit(solution)/shard_map/ppermute | solution.py:33
  5.1 7.0 %collective-permute-start.2 = (bf16[16,512]{1,0:T(8,128)(2,1)}, bf16[16,512]{1,0:T(8,128)(2,1)S(1)}, u32[]{:S(2)}, u32[]{:S(2)}) collective-permute-start(bf16[16,512]{1,0:T(8,128)(2,1)} %edge_rows.1), channel_id=1, source_target_pairs={{0,3},{1,2},{2,5},{3,4},{4,7},{5,6},{6,9},{7,8},{8,11},{9,10},{10,... | collective-permute-start | bytes 49160 | tf_op jit(solution)/shard_map/ppermute | solution.py:51
  6.5 5.5 %collective-permute-start.1 = (bf16[16,512]{1,0:T(8,128)(2,1)}, bf16[16,512]{1,0:T(8,128)(2,1)S(1)}, u32[]{:S(2)}, u32[]{:S(2)}) collective-permute-start(bf16[16,512]{1,0:T(8,128)(2,1)} %edge_rows.1), channel_id=1, source_target_pairs={{0,2},{2,4},{4,6},{6,8},{8,10},{10,12},{12,14},{14,16},{16,18},{18... | collective-permute-start | bytes 49160 | tf_op jit(solution)/shard_map/ppermute | solution.py:28
  10.5 14.3 %collective-permute-start.4 = (bf16[256,512]{1,0:T(8,128)(2,1)}, bf16[256,512]{1,0:T(8,128)(2,1)S(1)}, u32[]{:S(2)}, u32[]{:S(2)}) collective-permute-start(bf16[256,512]{1,0:T(8,128)(2,1)} %param.25), channel_id=1, source_target_pairs={{0,1},{1,0},{2,3},{3,2},{4,5},{5,4},{6,7},{7,6},{8,9},{9,8},{10,11... | collective-permute-start | bytes 786440 | tf_op jit(solution)/shard_map/ppermute | solution.py:33
  15.3 9.5 %copy-start.21 = (bf16[256,512]{1,0:T(8,128)(2,1)S(1)}, bf16[256,512]{1,0:T(8,128)(2,1)}, u32[]{:S(2)}) copy-start(bf16[256,512]{1,0:T(8,128)(2,1)} %param.25) | copy-start | bytes 786436
  23.8 4.9 %collective-permute-start.3 = (f32[96,256]{1,0:T(8,128)}, f32[96,256]{1,0:T(8,128)S(1)}, u32[]{:S(2)}, u32[]{:S(2)}) collective-permute-start(f32[96,256]{1,0:T(8,128)} %get-tuple-element.66.selected_ref), channel_id=1, source_target_pairs={{0,1},{1,0},{2,3},{3,2},{4,5},{5,4},{6,7},{7,6},{8,9},{9,8},{10,11... | collective-permute-start | bytes 294920 | tf_op jit(solution)/shard_map/ppermute | solution.py:33
  40.0 1.7 collective-permute-start.5
  44.3 6.5 %collective-permute-start.6 = (f32[40,1024]{1,0:T(8,128)}, f32[40,1024]{1,0:T(8,128)S(1)}, u32[]{:S(2)}, u32[]{:S(2)}) collective-permute-start(f32[40,1024]{1,0:T(8,128)} %get-tuple-element.70.own_ref), channel_id=1, source_target_pairs={{0,4},{2,6},{4,0},{6,2},{8,12},{10,14},{12,8},{14,10},{16,20},{18,... | collective-permute-start | bytes 491528 | tf_op jit(solution)/shard_map/ppermute | solution.py:33
  53.3 6.8 %collective-permute-start.7 = (f32[16,1024]{1,0:T(8,128)}, f32[16,1024]{1,0:T(8,128)S(1)}, u32[]{:S(2)}, u32[]{:S(2)}) collective-permute-start(f32[16,1024]{1,0:T(8,128)} %get-tuple-element.73), channel_id=1, source_target_pairs={{0,8},{2,10},{4,12},{6,14},{8,16},{10,18},{12,20},{14,22},{16,24},... | collective-permute-start | bytes 196616 | tf_op jit(solution)/shard_map/ppermute | solution.py:28
  57.9 13.2 %collective-permute-start.9 = (f32[16,1024]{1,0:T(8,128)}, f32[16,1024]{1,0:T(8,128)S(1)}, u32[]{:S(2)}, u32[]{:S(2)}) collective-permute-start(f32[16,1024]{1,0:T(8,128)} %get-tuple-element.78), channel_id=1, source_target_pairs={{8,0},{10,2},{12,4},{14,6},{16,8},{18,10},{20,12},{22,14},{24,16},... | collective-permute-start | bytes 196616 | tf_op jit(solution)/shard_map/ppermute | solution.py:28
  75.3 4.5 %collective-permute-start.10 = (bf16[1024,1024]{1,0:T(8,128)(2,1)}, bf16[1024,1024]{1,0:T(8,128)(2,1)}, u32[]{:S(2)}, u32[]{:S(2)}) collective-permute-start(bf16[1024,1024]{1,0:T(8,128)(2,1)} %early_send.1), channel_id=1, source_target_pairs={{0,2},{2,0},{4,6},{6,4},{8,10},{10,8},{12,14},{14,12},{16,18},{18,... | collective-permute-start | bytes 6291464 | tf_op jit(solution)/shard_map/ppermute | solution.py:33
  79.8 5.8 %copy-start.6 = (f32[256,512]{1,0:T(8,128)S(1)}, f32[256,512]{1,0:T(8,128)}, u32[]{:S(2)}) copy-start(f32[256,512]{1,0:T(8,128)} %slice_select_fusion.1.rest_0_.second_wait) | copy-start | bytes 1572868
  85.0 16.6 %collective-permute-start.11 = (bf16[512,1024]{1,0:T(8,128)(2,1)}, bf16[512,1024]{1,0:T(8,128)(2,1)S(1)}, u32[]{:S(2)}, u32[]{:S(2)}) collective-permute-start(bf16[512,1024]{1,0:T(8,128)(2,1)} %get-tuple-element.81.first_wait), channel_id=1, source_target_pairs={{0,4},{2,10},{4,0},{6,14},{8,12},{10,2},{12,8},{14,6},{16,20},{18,... | collective-permute-start | bytes 3145736 | tf_op jit(solution)/shard_map/ppermute | solution.py:112
  85.6 40.7 %collective-permute-start.8 = (f32[256,512]{1,0:T(8,128)S(1)}, f32[256,512]{1,0:T(8,128)S(1)}, u32[]{:S(2)}, u32[]{:S(2)}) collective-permute-start(f32[256,512]{1,0:T(8,128)S(1)} %copy-done.6), channel_id=1, source_target_pairs={{0,1},{1,0},{2,3},{3,2},{4,5},{5,4},{6,7},{7,6},{8,9},{9,8},{10,11... | collective-permute-start | bytes 1572872 | tf_op jit(solution)/shard_map/ppermute | solution.py:33
  105.8 29.5 %collective-permute-start.14 = (bf16[256,1024]{1,0:T(8,128)(2,1)}, bf16[256,1024]{1,0:T(8,128)(2,1)}, u32[]{:S(2)}, u32[]{:S(2)}) collective-permute-start(bf16[256,1024]{1,0:T(8,128)(2,1)} %get-tuple-element.84.first_wait), channel_id=1, source_target_pairs={{0,8},{2,18},{4,12},{6,22},{8,0},{10,26},{12,4},{14,30},{16,24},{1... | collective-permute-start | bytes 1572872 | tf_op jit(solution)/shard_map/ppermute | solution.py:112
  122.3 5.6 %collective-permute-start.12 = (f32[96,256]{1,0:T(8,128)}, f32[96,256]{1,0:T(8,128)S(1)}, u32[]{:S(2)}, u32[]{:S(2)}) collective-permute-start(f32[96,256]{1,0:T(8,128)} %get-tuple-element.85.select_grad_ref.refs_1_), channel_id=1, source_target_pairs={{0,1},{1,0},{2,3},{3,2},{4,5},{5,4},{6,7},{7,6},{8,9},{9,8},{10,11... | collective-permute-start | bytes 294920 | tf_op jit(solution)/shard_map/ppermute | solution.py:33
  124.8 10.5 %collective-permute-start.17 = (bf16[256,256]{1,0:T(8,128)(2,1)}, bf16[256,256]{1,0:T(8,128)(2,1)S(1)}, u32[]{:S(2)}, u32[]{:S(2)}) collective-permute-start(bf16[256,256]{1,0:T(8,128)(2,1)} %get-tuple-element.124), channel_id=1, source_target_pairs={{0,6},{2,4},{4,2},{6,0},{8,14},{10,12},{12,10},{14,8},{16,22},{18,... | collective-permute-start | bytes 393224 | tf_op jit(solution)/shard_map/ppermute | solution.py:33
  126.0 9.3 %collective-permute-start.16 = (bf16[256,256]{1,0:T(8,128)(2,1)}, bf16[256,256]{1,0:T(8,128)(2,1)S(1)}, u32[]{:S(2)}, u32[]{:S(2)}) collective-permute-start(bf16[256,256]{1,0:T(8,128)(2,1)} %get-tuple-element.125), channel_id=1, source_target_pairs={{0,2},{2,0},{4,6},{6,4},{8,10},{10,8},{12,14},{14,12},{16,18},{18,... | collective-permute-start | bytes 393224 | tf_op jit(solution)/shard_map/ppermute | solution.py:33
  126.3 1.6 copy-start.13
  126.3 9.0 %collective-permute-start.15 = (bf16[256,256]{1,0:T(8,128)(2,1)}, bf16[256,256]{1,0:T(8,128)(2,1)S(1)}, u32[]{:S(2)}, u32[]{:S(2)}) collective-permute-start(bf16[256,256]{1,0:T(8,128)(2,1)} %get-tuple-element.126), channel_id=1, source_target_pairs={{0,4},{2,6},{4,0},{6,2},{8,12},{10,14},{12,8},{14,10},{16,20},{18,... | collective-permute-start | bytes 393224 | tf_op jit(solution)/shard_map/ppermute | solution.py:33
  128.6 6.5 %copy-start.38 = (f32[256,1]{1,0:T(8,128)S(1)}, f32[256,1]{1,0:T(8,128)}, u32[]{:S(2)}) copy-start(f32[256,1]{1,0:T(8,128)} %get-tuple-element.75) | copy-start | bytes 3076
  133.4 10.8 %copy-start.12 = (bf16[256,1024]{1,0:T(8,128)(2,1)S(1)}, bf16[256,1024]{1,0:T(8,128)(2,1)}, u32[]{:S(2)}) copy-start(bf16[256,1024]{1,0:T(8,128)(2,1)} %get-tuple-element.80.gate_grad_ref) | copy-start | bytes 1572868
  133.4 7.6 %collective-permute-start.13 = (f32[8,1024]{1,0:T(8,128)}, f32[8,1024]{1,0:T(8,128)S(1)}, u32[]{:S(2)}, u32[]{:S(2)}) collective-permute-start(f32[8,1024]{1,0:T(8,128)} %get-tuple-element.91), channel_id=1, source_target_pairs={{2,0},{4,2},{6,4},{8,6},{10,8},{12,10},{14,12},{16,14},{18,16},{20... | collective-permute-start | bytes 98312 | tf_op jit(solution)/shard_map/ppermute | solution.py:28
  138.3 10.4 %collective-permute-start.20 = (bf16[128,1024]{1,0:T(8,128)(2,1)}, bf16[128,1024]{1,0:T(8,128)(2,1)}, u32[]{:S(2)}, u32[]{:S(2)}) collective-permute-start(bf16[128,1024]{1,0:T(8,128)(2,1)} %get-tuple-element.94.rest_0_), channel_id=1, source_target_pairs={{0,16},{2,6},{4,20},{6,2},{8,24},{10,14},{12,28},{14,10},{16,0},{1... | collective-permute-start | bytes 786440 | tf_op jit(solution)/shard_map/ppermute | solution.py:112
  143.1 18.9 %collective-permute-start.22 = (bf16[256,1024]{1,0:T(8,128)(2,1)}, bf16[256,1024]{1,0:T(8,128)(2,1)S(1)}, u32[]{:S(2)}, u32[]{:S(2)}) collective-permute-start(bf16[256,1024]{1,0:T(8,128)(2,1)} %patched.1.rest_0_.own_ref), channel_id=1, source_target_pairs={{0,4},{2,6},{4,0},{6,2},{8,12},{10,14},{12,8},{14,10},{16,20},{18,... | collective-permute-start | bytes 1572872 | tf_op jit(solution)/shard_map/ppermute | solution.py:33
  148.2 16.9 %copy-start.4 = (f32[256,1024]{1,0:T(8,128)}, f32[256,1024]{1,0:T(8,128)S(1)}, u32[]{:S(2)}) copy-start(f32[256,1024]{1,0:T(8,128)S(1)} %fusion.10) | copy-start | bytes 3145732
  148.2 6.9 %copy-start.42 = (f32[1024]{0:T(1024)S(1)}, f32[1024]{0:T(1024)}, u32[]{:S(2)}) copy-start(f32[1024]{0:T(1024)} %param.14) | copy-start | bytes 12292
  150.6 12.3 %copy-start.7 = (bf16[256,1024]{1,0:T(8,128)(2,1)S(1)}, bf16[256,1024]{1,0:T(8,128)(2,1)}, u32[]{:S(2)}) copy-start(bf16[256,1024]{1,0:T(8,128)(2,1)} %patched.1.rest_0_.own_ref) | copy-start | bytes 1572868
  152.8 4.2 %collective-permute-start.23 = (bf16[64,1024]{1,0:T(8,128)(2,1)}, bf16[64,1024]{1,0:T(8,128)(2,1)S(1)}, u32[]{:S(2)}, u32[]{:S(2)}) collective-permute-start(bf16[64,1024]{1,0:T(8,128)(2,1)} %get-tuple-element.99), channel_id=1, source_target_pairs={{0,2},{2,0},{4,6},{6,4},{8,10},{10,8},{12,14},{14,12},{16,18},{18,... | collective-permute-start | bytes 393224 | tf_op jit(solution)/shard_map/ppermute | solution.py:33
  152.8 6.6 %collective-permute-start.24 = (bf16[64,1024]{1,0:T(8,128)(2,1)}, bf16[64,1024]{1,0:T(8,128)(2,1)S(1)}, u32[]{:S(2)}, u32[]{:S(2)}) collective-permute-start(bf16[64,1024]{1,0:T(8,128)(2,1)} %get-tuple-element.100), channel_id=1, source_target_pairs={{0,4},{2,6},{4,0},{6,2},{8,12},{10,14},{12,8},{14,10},{16,20},{18,... | collective-permute-start | bytes 393224 | tf_op jit(solution)/shard_map/ppermute | solution.py:33
  154.9 7.1 %collective-permute-start.25 = (bf16[64,1024]{1,0:T(8,128)(2,1)}, bf16[64,1024]{1,0:T(8,128)(2,1)S(1)}, u32[]{:S(2)}, u32[]{:S(2)}) collective-permute-start(bf16[64,1024]{1,0:T(8,128)(2,1)} %get-tuple-element.101), channel_id=1, source_target_pairs={{0,6},{2,4},{4,2},{6,0},{8,14},{10,12},{12,10},{14,8},{16,22},{18,... | collective-permute-start | bytes 393224 | tf_op jit(solution)/shard_map/ppermute | solution.py:33
  157.0 5.0 %copy-start.31 = (bf16[64,1024]{1,0:T(8,128)(2,1)}, bf16[64,1024]{1,0:T(8,128)(2,1)S(1)}, u32[]{:S(2)}) copy-start(bf16[64,1024]{1,0:T(8,128)(2,1)S(1)} %collective-permute-done.23.refs_2_.first_ref) | copy-start | bytes 393220
  159.5 2.6 copy-start.32
  162.9 4.3 %copy-start.41 = (f32[1024]{0:T(1024)S(1)}, f32[1024]{0:T(1024)}, u32[]{:S(2)}) copy-start(f32[1024]{0:T(1024)} %get-tuple-element.116) | copy-start | bytes 12292
  162.9 6.3 %copy-start.11 = (bf16[128,1024]{1,0:T(8,128)(2,1)S(1)}, bf16[128,1024]{1,0:T(8,128)(2,1)}, u32[]{:S(2)}) copy-start(bf16[128,1024]{1,0:T(8,128)(2,1)} %settled.1.wait_ref.held_ref) | copy-start | bytes 786436
  165.0 16.1 %collective-permute-start.26 = (bf16[512,1024]{1,0:T(8,128)(2,1)}, bf16[512,1024]{1,0:T(8,128)(2,1)}, u32[]{:S(2)}, u32[]{:S(2)}) collective-permute-start(bf16[512,1024]{1,0:T(8,128)(2,1)} %pad_maximum_fusion), channel_id=1, source_target_pairs={{0,2},{2,0},{4,6},{6,4},{8,10},{10,8},{12,14},{14,12},{16,18},{18,... | collective-permute-start | bytes 3145736 | tf_op jit(solution)/shard_map/ppermute | solution.py:33
  166.0 26.2 %collective-permute-start.18 = (f32[256,512]{1,0:T(8,128)}, f32[256,512]{1,0:T(8,128)S(1)}, u32[]{:S(2)}, u32[]{:S(2)}) collective-permute-start(f32[256,512]{1,0:T(8,128)} %slice_select_fusion), channel_id=1, source_target_pairs={{0,1},{1,0},{2,3},{3,2},{4,5},{5,4},{6,7},{7,6},{8,9},{9,8},{10,11... | collective-permute-start | bytes 1572872 | tf_op jit(solution)/shard_map/ppermute | solution.py:33
  167.1 13.4 %collective-permute-start.27 = (f32[1,1024]{1,0:T(1,128)S(1)}, f32[1,1024]{1,0:T(1,128)S(1)}, u32[]{:S(2)}, u32[]{:S(2)}) collective-permute-start(f32[1,1024]{1,0:T(1,128)S(1)} %bitcast.35), channel_id=1, source_target_pairs={{0,1},{1,0},{2,3},{3,2},{4,5},{5,4},{6,7},{7,6},{8,9},{9,8},{10,11... | collective-permute-start | bytes 12296 | tf_op jit(solution)/shard_map/ppermute | solution.py:33
  168.1 13.1 %collective-permute-start.19 = (f32[1,256]{1,0:T(1,128)S(1)}, f32[1,256]{1,0:T(1,128)S(1)}, u32[]{:S(2)}, u32[]{:S(2)}) collective-permute-start(f32[1,256]{1,0:T(1,128)S(1)} %bitcast.44), channel_id=1, source_target_pairs={{0,1},{1,0},{2,3},{3,2},{4,5},{5,4},{6,7},{7,6},{8,9},{9,8},{10,11... | collective-permute-start | bytes 3080 | tf_op jit(solution)/shard_map/ppermute | solution.py:33
  169.2 20.5 %collective-permute-start.21 = (bf16[128,1024]{1,0:T(8,128)(2,1)S(1)}, bf16[128,1024]{1,0:T(8,128)(2,1)S(1)}, u32[]{:S(2)}, u32[]{:S(2)}) collective-permute-start(bf16[128,1024]{1,0:T(8,128)(2,1)S(1)} %copy-done.11), channel_id=1, source_target_pairs={{0,16},{2,6},{4,20},{6,2},{8,24},{10,14},{12,28},{14,10},{16,0},{1... | collective-permute-start | bytes 786440 | tf_op jit(solution)/shard_map/ppermute | solution.py:112
  185.2 19.2 %copy-start.18 = (f32[80,1024]{1,0:T(8,128)S(1)}, f32[80,1024]{1,0:T(8,128)}, u32[]{:S(2)}) copy-start(f32[80,1024]{1,0:T(8,128)} %get-tuple-element.103.rest_0_) | copy-start | bytes 983044
  185.2 8.5 %collective-permute-start.29 = (bf16[80,1024]{1,0:T(8,128)(2,1)}, bf16[80,1024]{1,0:T(8,128)(2,1)S(1)}, u32[]{:S(2)}, u32[]{:S(2)}) collective-permute-start(bf16[80,1024]{1,0:T(8,128)(2,1)} %get-tuple-element.104), channel_id=1, source_target_pairs={{0,8},{2,10},{4,12},{6,14},{8,0},{10,2},{12,4},{14,6},{16,24},{18,... | collective-permute-start | bytes 491528 | tf_op jit(solution)/shard_map/ppermute | solution.py:33
  185.4 18.9 %collective-permute-start.30 = (bf16[80,1024]{1,0:T(8,128)(2,1)}, bf16[80,1024]{1,0:T(8,128)(2,1)S(1)}, u32[]{:S(2)}, u32[]{:S(2)}) collective-permute-start(bf16[80,1024]{1,0:T(8,128)(2,1)} %get-tuple-element.105), channel_id=1, source_target_pairs={{0,16},{2,18},{4,20},{6,22},{8,24},{10,26},{12,28},{14,30},{16,0},... | collective-permute-start | bytes 491528 | tf_op jit(solution)/shard_map/ppermute | solution.py:33
  188.8 15.5 %collective-permute-start.31 = (bf16[80,1024]{1,0:T(8,128)(2,1)}, bf16[80,1024]{1,0:T(8,128)(2,1)}, u32[]{:S(2)}, u32[]{:S(2)}) collective-permute-start(bf16[80,1024]{1,0:T(8,128)(2,1)} %get-tuple-element.106), channel_id=1, source_target_pairs={{0,24},{2,26},{4,28},{6,30},{8,16},{10,18},{12,20},{14,22},{16,8},... | collective-permute-start | bytes 491528 | tf_op jit(solution)/shard_map/ppermute | solution.py:33
  192.2 31.7 %collective-permute-start.28 = (bf16[256,1024]{1,0:T(8,128)(2,1)}, bf16[256,1024]{1,0:T(8,128)(2,1)S(1)}, u32[]{:S(2)}, u32[]{:S(2)}) collective-permute-start(bf16[256,1024]{1,0:T(8,128)(2,1)} %unfolded.3.refs_2_.held_ref), channel_id=1, source_target_pairs={{0,8},{2,18},{4,12},{6,22},{8,0},{10,26},{12,4},{14,30},{16,24},{1... | collective-permute-start | bytes 1572872 | tf_op jit(solution)/shard_map/ppermute | solution.py:112
  192.2 1.5 copy-start.15
  205.5 18.4 %copy-start.22 = (bf16[80,1024]{1,0:T(8,128)(2,1)}, bf16[80,1024]{1,0:T(8,128)(2,1)S(1)}, u32[]{:S(2)}) copy-start(bf16[80,1024]{1,0:T(8,128)(2,1)S(1)} %pad_maximum_fusion.5.rest_0_) | copy-start | bytes 491524
  205.5 17.7 %collective-permute-start.34 = (bf16[80,1024]{1,0:T(8,128)(2,1)S(1)}, bf16[80,1024]{1,0:T(8,128)(2,1)S(1)}, u32[]{:S(2)}, u32[]{:S(2)}) collective-permute-start(bf16[80,1024]{1,0:T(8,128)(2,1)S(1)} %pad_maximum_fusion.5.rest_0_), channel_id=1, source_target_pairs={{0,16},{2,18},{4,20},{6,22},{8,24},{10,26},{12,28},{14,30},{16,0},... | collective-permute-start | bytes 491528 | tf_op jit(solution)/shard_map/ppermute | solution.py:33
  213.1 10.2 %collective-permute-start.33 = (bf16[80,1024]{1,0:T(8,128)(2,1)S(1)}, bf16[80,1024]{1,0:T(8,128)(2,1)S(1)}, u32[]{:S(2)}, u32[]{:S(2)}) collective-permute-start(bf16[80,1024]{1,0:T(8,128)(2,1)S(1)} %pad_maximum_fusion.5.rest_0_), channel_id=1, source_target_pairs={{0,24},{2,26},{4,28},{6,30},{8,16},{10,18},{12,20},{14,22},{16,8},... | collective-permute-start | bytes 491528 | tf_op jit(solution)/shard_map/ppermute | solution.py:33
  214.5 12.4 %collective-permute-start.35 = (bf16[80,1024]{1,0:T(8,128)(2,1)S(1)}, bf16[80,1024]{1,0:T(8,128)(2,1)S(1)}, u32[]{:S(2)}, u32[]{:S(2)}) collective-permute-start(bf16[80,1024]{1,0:T(8,128)(2,1)S(1)} %pad_maximum_fusion.5.rest_0_), channel_id=1, source_target_pairs={{0,8},{2,10},{4,12},{6,14},{8,0},{10,2},{12,4},{14,6},{16,24},{18,... | collective-permute-start | bytes 491528 | tf_op jit(solution)/shard_map/ppermute | solution.py:33
  227.0 15.0 %collective-permute-start.32 = (bf16[512,1024]{1,0:T(8,128)(2,1)}, bf16[512,1024]{1,0:T(8,128)(2,1)S(1)}, u32[]{:S(2)}, u32[]{:S(2)}) collective-permute-start(bf16[512,1024]{1,0:T(8,128)(2,1)} %unfolded.4.refs_1_.held_ref), channel_id=1, source_target_pairs={{0,4},{2,10},{4,0},{6,14},{8,12},{10,2},{12,8},{14,6},{16,20},{18,... | collective-permute-start | bytes 3145736 | tf_op jit(solution)/shard_map/ppermute | solution.py:112
  229.7 20.0 %copy-start.47 = (f32[1,256]{1,0:T(1,128)S(1)}, f32[1,256]{1,0:T(1,128)}, u32[]{:S(2)}) copy-start(f32[1,256]{1,0:T(1,128)} %copy-done.46) | copy-start | bytes 3076
  229.7 20.0 %copy-start.5 = (f32[256,1024]{1,0:T(8,128)S(1)}, f32[256,1024]{1,0:T(8,128)}, u32[]{:S(2)}) copy-start(f32[256,1024]{1,0:T(8,128)} %copy-done.4) | copy-start | bytes 3145732
  229.7 20.0 %copy-start.10 = (bf16[256,512]{1,0:T(8,128)(2,1)S(1)}, bf16[256,512]{1,0:T(8,128)(2,1)}, u32[]{:S(2)}) copy-start(bf16[256,512]{1,0:T(8,128)(2,1)} %own_ref.1) | copy-start | bytes 786436
  229.7 20.0 %copy-start.14 = (f32[256,512]{1,0:T(8,128)S(1)}, f32[256,512]{1,0:T(8,128)}, u32[]{:S(2)}) copy-start(f32[256,512]{1,0:T(8,128)} %copy-done.13) | copy-start | bytes 1572868
  229.7 20.0 %copy-start.16 = (f32[256,512]{1,0:T(8,128)S(1)}, f32[256,512]{1,0:T(8,128)}, u32[]{:S(2)}) copy-start(f32[256,512]{1,0:T(8,128)} %copy-done.15) | copy-start | bytes 1572868
  229.7 7.4 %collective-permute-start.36 = (bf16[320,1024]{1,0:T(8,128)(2,1)}, bf16[320,1024]{1,0:T(8,128)(2,1)S(1)}, u32[]{:S(2)}, u32[]{:S(2)}) collective-permute-start(bf16[320,1024]{1,0:T(8,128)(2,1)} %pad_maximum_fusion.1.first_ref.rest_0_), channel_id=1, source_target_pairs={{0,2},{2,0},{4,6},{6,4},{8,10},{10,8},{12,14},{14,12},{16,18},{18,... | collective-permute-start | bytes 1966088 | tf_op jit(solution)/shard_map/ppermute | solution.py:33
  237.2 4.8 %copy-start.3 = (bf16[320,1024]{1,0:T(8,128)(2,1)}, bf16[320,1024]{1,0:T(8,128)(2,1)S(1)}, u32[]{:S(2)}) copy-start(bf16[320,1024]{1,0:T(8,128)(2,1)S(1)} %collective-permute-done.36.rest_0_.wait_ref.second_ref.rest_1_) | copy-start | bytes 1966084
  245.9 6.8 %collective-permute-start.37 = (bf16[1024,1024]{1,0:T(8,128)(2,1)}, bf16[1024,1024]{1,0:T(8,128)(2,1)S(1)}, u32[]{:S(2)}, u32[]{:S(2)}) collective-permute-start(bf16[1024,1024]{1,0:T(8,128)(2,1)} %unfolded.5.own_ref.own_gate), channel_id=1, source_target_pairs={{0,2},{2,0},{4,6},{6,4},{8,10},{10,8},{12,14},{14,12},{16,18},{18,... | collective-permute-start | bytes 6291464 | tf_op jit(solution)/shard_map/ppermute | solution.py:33
  248.7 17.0 %collective-permute-start.38 = (bf16[320,1024]{1,0:T(8,128)(2,1)}, bf16[320,1024]{1,0:T(8,128)(2,1)}, u32[]{:S(2)}, u32[]{:S(2)}) collective-permute-start(bf16[320,1024]{1,0:T(8,128)(2,1)} %pad_maximum_fusion.1.first_ref.rest_0_), channel_id=1, source_target_pairs={{0,4},{2,6},{4,0},{6,2},{8,12},{10,14},{12,8},{14,10},{16,20},{18,... | collective-permute-start | bytes 1966088 | tf_op jit(solution)/shard_map/ppermute | solution.py:33
  252.7 1.3 copy-start.2
  265.7 2.3 collective-permute-start.39
  268.8 6.4 %copy-start.1 = (bf16[1024,1024]{1,0:T(8,128)(2,1)S(1)}, bf16[1024,1024]{1,0:T(8,128)(2,1)}, u32[]{:S(2)}) copy-start(bf16[1024,1024]{1,0:T(8,128)(2,1)} %param.23) | copy-start | bytes 6291460
  (24 other events, 17.2 us)

commit v15 on v10

--- a/solution.py
+++ b/solution.py
@@ -356,7 +356,6 @@
     passed_ref,
     entering_ref,
     skip_ref,
-    wait_ref,
     gated_ref,
     gate_grad_ref,
     entry_ref,
@@ -399,7 +398,7 @@
 
 
 def scan_forward(
-    selected, other, step, act, projected, gated_grad, masks, decay_log, passed, entering, skip_gain, wait
+    selected, other, step, act, projected, gated_grad, masks, decay_log, passed, entering, skip_gain
 ):
     rows, width = step.shape
     count = decay_log.shape[0]
@@ -420,7 +419,6 @@
             column_spec(2 * count + 8),
             column_spec(count),
             column_spec(1),
-            pl.BlockSpec(memory_space=pl.ANY),
         ],
         [column_spec(rows), column_spec(rows), column_spec(count)],
         [
@@ -442,7 +440,6 @@
         passed,
         entering,
         skip_gain,
-        wait,
     )
 
 
@@ -796,7 +793,7 @@
     )(array, *waits)
 
 
-def patch_kernel(ids_ref, rows_ref, last_ref, next_ref, out_ref):
+def patch_kernel(ids_ref, rows_ref, last_ref, next_ref, *rest):
     count = ids_ref.shape[0]
     place = lax.broadcasted_iota(jnp.int32, (8, 1), 0)
     same = jnp.zeros((8, 1), f32)
@@ -805,23 +802,24 @@
         same = same + jnp.where(place == 7 - lag, here, 0.0)
     total = last_ref[...] + next_ref[...] * same
     rows = rows_ref[...].astype(f32)
-    out_ref[...] = jnp.concatenate([rows[: halo - 8], total]).astype(bf16)
-
-
-def patched(ids, grads, last, following):
+    rest[-1][...] = jnp.concatenate([rows[: halo - 8], total]).astype(bf16)
+
+
+def patched(ids, grads, last, following, *waits):
     rows, width = grads.shape
     block = pl.BlockSpec((halo, width), lambda j: (rows // halo - 1, 0))
     edge = pl.BlockSpec((8, width), lambda j: (0, 0))
     return pl.pallas_call(
         patch_kernel,
         grid=(1,),
-        in_specs=[pl.BlockSpec(memory_space=pltpu.SMEM), block, edge, edge],
+        in_specs=[pl.BlockSpec(memory_space=pltpu.SMEM), block, edge, edge]
+        + [pl.BlockSpec(memory_space=pl.ANY)] * len(waits),
         out_specs=block,
         out_shape=jax.ShapeDtypeStruct((rows, width), bf16),
         input_output_aliases={1: 0},
         cost_estimate=tiny_cost,
         name="patched",
-    )(ids, grads, last, following)
+    )(ids, grads, last, following, *waits)
 
 
 def edge_kernel(ids_ref, tokens_ref, out_ref):
@@ -855,7 +853,7 @@
 block_rows, used_rows = 16, 12
 
 
-def small_kernel(place_ref, scan_ref, conv_ref, keep_ref, *rest):
+def small_kernel(place_ref, scan_ref, conv_ref, wait_ref, keep_ref, *rest):
     *sends_refs, rows, blocks = rest
     rows[...] = jnp.zeros(rows.shape, f32)
     rows[: scan_ref.shape[0], :] = scan_ref[...]
@@ -875,12 +873,13 @@
             sends_refs[n - 1][...] = block.astype(bf16)
 
 
-def small_quarters(place, scan_small, conv_small):
+def small_quarters(place, scan_small, conv_small, wait):
     width = scan_small.shape[1]
     return pl.pallas_call(
         small_kernel,
         in_specs=[pl.BlockSpec(memory_space=pltpu.SMEM)]
-        + [pl.BlockSpec(memory_space=pltpu.VMEM)] * 2,
+        + [pl.BlockSpec(memory_space=pltpu.VMEM)] * 2
+        + [pl.BlockSpec(memory_space=pl.ANY)],
         out_shape=[jax.ShapeDtypeStruct((4 * block_rows, width), f32)]
         + [jax.ShapeDtypeStruct((4 * block_rows, width), bf16)] * 3,
         scratch_shapes=[
@@ -889,7 +888,7 @@
         ],
         cost_estimate=tiny_cost,
         name="small_quarters",
-    )(place, scan_small, conv_small)
+    )(place, scan_small, conv_small, wait)
 
 
 def quarter_kernel(
@@ -897,7 +896,6 @@
     own_ref,
     near_ref,
     far_ref,
-    last_ref,
     normed_0,
     normed_1,
     normed_2,
@@ -910,9 +908,10 @@
 ):
     keep_ref, *sends_refs, piece, small = rest[-6:]
     total = None
-    grads = (own_ref, near_ref, far_ref, last_ref)
+    tokens = own_ref.shape[0]
+    grads = (own_ref[...], near_ref[...], far_ref[:tokens, :], far_ref[tokens:, :])
     for left, right in zip((normed_0, normed_1, normed_2, normed_3), grads):
-        part = lax.dot_general(left[...], right[...], contract_first, preferred_element_type=f32)
+        part = lax.dot_general(left[...], right, contract_first, preferred_element_type=f32)
         total = part if total is None else total + part
     piece[...] = total
     small[...] = small_ref[...] + sum(
@@ -931,7 +930,7 @@
             sends_refs[n - 1][rows:, :] = small_rows.astype(bf16)
 
 
-def inner_quarter(place, own, near, far, last, normed, smalls, waits):
+def inner_quarter(place, own, near, far, normed, smalls, waits):
     width = own.shape[1]
     quarter = normed[0].shape[1]
     spare = smalls[0].shape[0]
@@ -939,7 +938,7 @@
     return pl.pallas_call(
         quarter_kernel,
         in_specs=[pl.BlockSpec(memory_space=pltpu.SMEM)]
-        + [pl.BlockSpec(memory_space=pltpu.VMEM)] * 12
+        + [pl.BlockSpec(memory_space=pltpu.VMEM)] * 11
         + [pl.BlockSpec(memory_space=pl.ANY)] * len(waits),
         out_shape=[jax.ShapeDtypeStruct((rows, width), f32)]
         + [jax.ShapeDtypeStruct((rows, width), bf16)] * 3,
@@ -947,7 +946,7 @@
         compiler_params=pltpu.CompilerParams(vmem_limit_bytes=vmem_bytes),
         cost_estimate=tiny_cost,
         name="inner_quarter",
-    )(place, own, near, far, last, *normed, *smalls, *waits)
+    )(place, own, near, far, *normed, *smalls, *waits)
 
 
 def join_kernel(place_ref, gate_ref, first_ref, second_ref, *rest, small_rows):
@@ -1150,8 +1149,8 @@
         passed,
         entering,
         skip_gain[None],
-        returning,
-    )
+    )
+    gated = after(gated, returning)
     products = (
         lax.dot_general(gated, cot_whole, contract_first, preferred_element_type=f32).astype(bf16),
         lax.dot_general(normed, gate_grad, contract_first, preferred_element_type=f32).astype(bf16),
@@ -1166,10 +1165,6 @@
 
     def after_forward(products):
         whole = whole_low.astype(f32)
-        normed_four = quarter_of_four(normed)
-        out_part = jnp.dot(gated, out_weight, preferred_element_type=f32)
-        out_mine, out_other = narrow_halves(out_part)
-        out_theirs = swapped(out_other, "narrow", 1)
         act_grad, select_grad, scan_small = scan_backward(
             selected,
             other_selected,
@@ -1186,7 +1181,7 @@
             skip_gain[None],
             step_weight,
         )
-        layer_out = (tokens.astype(f32) + (out_mine + out_theirs)).astype(bf16)
+        normed_four = quarter_of_four(after(normed, select_grad))
         inner_main, before, last, conv_small = convolve_grad(
             select_grad,
             swapped(select_grad, "narrow", 1),
@@ -1197,42 +1192,46 @@
             projected,
             conv_weight,
             masks,
-            [out_theirs, *normed_four],
+            [],
         )
-        inner_grad = patched(segment_ids, inner_main, last, passed_along(before, "wide", -1))
+        following = passed_along(before, "wide", -1)
+        inner_grad = patched(segment_ids, inner_main, last, following, *normed_four)
         near = swapped(inner_grad, "wide", 2)
-        far = swapped(inner_grad, "wide", 1)
-        keep, *sends = small_quarters(four_place, scan_small, conv_small)
+        keep, *sends = small_quarters(four_place, scan_small, conv_small, inner_grad)
         smalls = [keep] + [swapped(sends[n - 1], "wide", n) for n in (1, 2, 3)]
         normed_part = jnp.einsum(
             "cte,dce->td", jnp.stack([inner_grad, gate_grad]), in_weight, preferred_element_type=f32
         )
         gain_part = jnp.sum(normed_part * whole * inverse, axis=0, keepdims=True)
         row_part = jnp.sum(normed_part * norm_gain * whole, axis=1)[None]
-        normed_mine, normed_other = narrow_halves(normed_part)
+        near = after(near, gain_part, *smalls[1:])
+        far = swapped(jnp.concatenate([inner_grad, near]), "wide", 1)
+        first_bits, *more_bits = group_bits(2)
+        gain_sum = gain_part + swapped(gain_part, "narrow", 1)
+        for bit in (bit for bits in more_bits for bit in bits):
+            gain_sum = gain_sum + swapped(gain_sum, "wide", bit)
         row_theirs = swapped(row_part, "narrow", 1)
-        normed_theirs = swapped(normed_other, "narrow", 1)
-        near = after(near, *smalls[1:])
         keep, *sends = inner_quarter(
             (wide_place >> 2 & 3)[None],
             inner_grad,
             near,
             far,
-            swapped(near, "wide", 1),
             normed_four,
             smalls,
-            [row_theirs],
+            [gain_sum, row_theirs],
         )
+        normed_mine, normed_other = narrow_halves(normed_part)
+        normed_theirs = swapped(after(normed_other, keep), "narrow", 1)
+        out_part = jnp.dot(gated, out_weight, preferred_element_type=f32)
+        out_mine, out_other = narrow_halves(out_part)
+        out_theirs = swapped(after(out_other, keep), "narrow", 1)
+        layer_out = (tokens.astype(f32) + (out_mine + out_theirs)).astype(bf16)
         row_sum = (row_part + row_theirs).reshape(rows, 1)
         gain_mine = jnp.where(right_half, norm_gain[features:], norm_gain[:features])
         whole_grad = inverse * (gain_mine * (normed_mine + normed_theirs)) - tokens.astype(f32) * (
             inverse * inverse * inverse
         ) * (row_sum / (2 * features))
         tokens_grad = (whole_grad + cotangent.astype(f32)).astype(bf16)
-        first_bits, *more_bits = group_bits(2)
-        gain_sum = gain_part + swapped(gain_part, "narrow", 1)
-        for bit in (bit for bits in more_bits for bit in bits):
-            gain_sum = gain_sum + swapped(gain_sum, "wide", bit)
         held = keep
         for n, flip in enumerate(flips(first_bits)[1:]):
             held = held + swapped(sends[n], "wide", flip).astype(f32)

time: 259 us -> 247 us (0.954)
  waiting for transfers between devices: 83.6 us -> 68 us
  starting transfers between devices: 42.6 us -> 45.2 us
    ppermute x28 -> x27, waiting for transfers between devices: 76.5 us -> 54.3 us  [swapped(): return lax.ppermute(array, axis, [(i, i ^ bit) for i in range(peers)])]
    psum x1, waiting for transfers between devices: 0.01 us -> 10.7 us  [local(): out_sum, gate_sum = lax.psum(products, 'wide')]
    ppermute x4, waiting for transfers between devices: 7.08 us -> 2.92 us  [passed_along(): return lax.ppermute(array, axis, pairs)]
    ppermute x28 -> x27, starting transfers between devices: 30 us -> 32.5 us  [swapped(): return lax.ppermute(array, axis, [(i, i ^ bit) for i in range(peers)])]
    unnamed x42 -> x44, local copies, waits for them, and re-layouts: 5.24 us -> 5.2 us
  transfers between devices with their start and end apart: 34 -> 33, of which waited for: 17 -> 17; matrix products, arithmetic and copies ran while one was open for 9% -> 11% of each run, Pallas kernels for 18% -> 23%
where the time goes in v15:
time: 247 us; the launch traced here: 246 us
  Pallas kernels  75.9 us (31%)
  waiting for transfers between devices  68 us (28%)
  starting transfers between devices  45.2 us (18%)
  matrix products  17.6 us (7%)
  between operations  14.9 us (6%)
  other arithmetic  12 us (5%)
  local copies, waits for them, and re-layouts  11.8 us (5%)
    ppermute x27, waiting for transfers between devices, swapped(): return lax.ppermute(array, axis, [(i, i ^ bit) for i in range(peers)])  54.3 us
    pallas_call x5, Pallas kernels, call(): pl.pallas_call(kernel, grid=(width // scan_width,), in_specs=in_specs, ou...  50.5 us
    ppermute x27, starting transfers between devices, swapped(): return lax.ppermute(array, axis, [(i, i ^ bit) for i in range(peers)])  32.5 us
    ppermute x4, starting transfers between devices, passed_along(): return lax.ppermute(array, axis, pairs)  11.3 us
    pallas_call x2, Pallas kernels, joined(): pl.pallas_call(functools.partial(join_kernel, small_rows=small_rows), gri...  10.8 us
    psum x1, waiting for transfers between devices, local(): out_sum, gate_sum = lax.psum(products, 'wide')  10.7 us
    dot_general x1, matrix products, after_forward(): jnp.einsum('cte,dce->td', jnp.stack([inner_grad, gate_grad]), in_weight,...  5.86 us
    unnamed x44, local copies, waits for them, and re-layouts  5.2 us
  transfers between devices with their start and end apart: 33, of which 17 were waited for; matrix products, arithmetic and copies ran while one was open for 11% of the time, Pallas kernels for 23%

profile of v15, /device:TPU:0, one launch (start us, length us, event | category | flops | bytes accessed | tf_op | source)
XLA Modules:
  0.0 245.7 jit_solution(12337291139919317853)
XLA Ops:
  7.2 3.0 %collective-permute-start.20 = (bf16[256,512]{1,0:T(8,128)(2,1)}, bf16[256,512]{1,0:T(8,128)(2,1)S(1)}, u32[]{:S(2)}, u32[]{:S(2)}) collective-permute-start(bf16[256,512]{1,0:T(8,128)(2,1)} %own_ref.1), channel_id=1, source_target_pairs={{0,1},{1,0},{2,3},{3,2},{4,5},{5,4},{6,7},{7,6},{8,9},{9,8},{10,11... | collective-permute-start | bytes 786440 | tf_op jit(solution)/shard_map/ppermute | solution.py:33
  10.3 1.4 edge_rows.1
  11.6 1.3 collective-permute-start.22
  13.0 4.0 %collective-permute-start.21 = (bf16[16,512]{1,0:T(8,128)(2,1)}, bf16[16,512]{1,0:T(8,128)(2,1)S(1)}, u32[]{:S(2)}, u32[]{:S(2)}) collective-permute-start(bf16[16,512]{1,0:T(8,128)(2,1)} %edge_rows.1), channel_id=1, source_target_pairs={{0,2},{2,4},{4,6},{6,8},{8,10},{10,12},{12,14},{14,16},{16,18},{18... | collective-permute-start | bytes 49160 | tf_op jit(solution)/shard_map/ppermute | solution.py:28
  17.0 1.6 collective-permute-start.24
  19.3 2.5 %normalized.1 = (bf16[256,1024]{1,0:T(8,128)(2,1)}, bf16[272,1024]{1,0:T(8,128)(2,1)}, bf16[256,1024]{1,0:T(8,128)(2,1)}, f32[256,1]{1,0:T(8,128)}, f32[256,128]{1,0:T(8,128)S(1)}) custom-call(bf16[256,512]{1,0:T(8,128)(2,1)} %own_ref.1, bf16[256,512]{1,0:T(8,128)(2,1)} %copy-done.30, bf16[16,512]{1,0:T(8,128)(2,1)} %copy-done.42, ...), custom_call_target="tpu_custom_call" | custom-call | flops 1 | bytes 1 | tf_op jit(solution)/shard_map/normalized/pallas_call | solution.py:768
  21.8 4.0 %fusion.25.inner_ref.gate_ref = bf16[2,272,1024]{2,1,0:T(8,128)(2,1)S(1)} fusion(bf16[1024,2,1024]{2,1,0:T(2,128)(2,1)} %param.17, bf16[272,1024]{1,0:T(8,128)(2,1)} %get-tuple-element.151), kind=kOutput, calls=%fused_computation.49 | convolution fusion | flops 1141407744 | bytes 5865472 | tf_op jit(solution)/shard_map/td,dce->cte/dot_general | solution.py:1117
  25.8 3.1 %convolve.1 = (f32[256,1024]{1,0:T(8,128)}, bf16[256,1024]{1,0:T(8,128)(2,1)S(1)}, f32[96,256]{1,0:T(8,128)S(1)}) custom-call(bf16[2,272,1024]{2,1,0:T(8,128)(2,1)S(1)} %fusion.25.inner_ref.gate_ref, f32[4,1024]{1,0:T(4,128)S(1)} %copy-done.36, f32[1,1024]{1,0:T(1,128)} %bitcast.46, bf16[96,1024]{1,0:T(8,128)(2,1)S(1)} %copy-done.18, ...), custom_call_target="tpu_custom_call" | custom-call | flops 1 | bytes 1 | tf_op jit(solution)/shard_map/convolve/pallas_call | solution.py:127
  28.9 0.9 collective-permute-start.23
  30.7 2.8 %collective-permute-done.23.other_ref = f32[96,256]{1,0:T(8,128)S(1)} collective-permute-done((f32[96,256]{1,0:T(8,128)S(1)}, f32[96,256]{1,0:T(8,128)S(1)}, u32[]{:S(2)}, u32[]{:S(2)}) %collective-permute-start.23) | collective-permute-done | bytes 98336 | tf_op jit(solution)/shard_map/ppermute | solution.py:33
  33.6 10.0 %scan_ends.1 = (f32[256,1024]{1,0:T(8,128)}, f32[256,1024]{1,0:T(8,128)}, f32[40,1024]{1,0:T(8,128)}) custom-call(f32[96,256]{1,0:T(8,128)S(1)} %get-tuple-element.153.selected_ref, f32[96,256]{1,0:T(8,128)S(1)} %collective-permute-done.23.other_ref, bf16[64,1024]{1,0:T(8,128)(2,1)S(1)} %copy-done.20, f32[1,1024]{1,0:T(1,128)} %bitcast.47, ...), custom_call_target="tpu_custom_call" | custom-call | flops 1 | bytes 1 | tf_op jit(solution)/shard_map/scan_ends/pallas_call | solution.py:127
  43.7 1.6 collective-permute-done.25.other_ref
  46.0 1.8 carry_round.2
  47.9 1.7 collective-permute-start.26
  49.6 4.8 %collective-permute-done.26.other_ref = f32[40,1024]{1,0:T(8,128)S(1)} collective-permute-done((f32[40,1024]{1,0:T(8,128)}, f32[40,1024]{1,0:T(8,128)S(1)}, u32[]{:S(2)}, u32[]{:S(2)}) %collective-permute-start.26) | collective-permute-done | bytes 163872 | tf_op jit(solution)/shard_map/ppermute | solution.py:33
  55.0 1.8 carry_round.3
  56.8 4.6 %collective-permute-start.27 = (f32[16,1024]{1,0:T(8,128)}, f32[16,1024]{1,0:T(8,128)S(1)}, u32[]{:S(2)}, u32[]{:S(2)}) collective-permute-start(f32[16,1024]{1,0:T(8,128)} %get-tuple-element.161), channel_id=1, source_target_pairs={{0,8},{2,10},{4,12},{6,14},{8,16},{10,18},{12,20},{14,22},{16,24},... | collective-permute-start | bytes 196616 | tf_op jit(solution)/shard_map/ppermute | solution.py:28
  61.4 1.3 collective-permute-start.28
  64.2 9.7 %scan_forward.1 = (bf16[256,1024]{1,0:T(8,128)(2,1)S(1)}, bf16[256,1024]{1,0:T(8,128)(2,1)}, f32[16,1024]{1,0:T(8,128)}) custom-call(f32[96,256]{1,0:T(8,128)S(1)} %get-tuple-element.153.selected_ref, f32[96,256]{1,0:T(8,128)} %copy-done.17, f32[256,1024]{1,0:T(8,128)} %get-tuple-element.156.step_ref, bf16[256,1024]{1,0:T(8,128)(2,1)S(1)} %get-tuple-element.154.act_ref, ...), custom_call_target="tpu_custom_call" | custom-call | flops 1 | bytes 1 | tf_op jit(solution)/shard_map/scan_forward/pallas_call | solution.py:127
  74.6 3.2 %convolution_convert_fusion = bf16[1024,1024]{1,0:T(8,128)(2,1)} fusion(bf16[256,1024]{1,0:T(8,128)(2,1)S(1)} %after.10, bf16[256,512]{1,0:T(8,128)(2,1)} %copy-done.11, bf16[256,512]{1,0:T(8,128)(2,1)} %copy-done.10), kind=kOutput, calls=%fused_computation.46 | convolution fusion | flops 538968064 | bytes 3145728 | tf_op jit(solution)/shard_map/dot_general | solution.py:1155
  77.8 2.1 convolution_convert_fusion.1
  79.8 1.2 slice.24
  81.7 125.3 %conditional.1 = (bf16[320,1024]{1,0:T(8,128)(2,1)}, bf16[256,512]{1,0:T(8,128)(2,1)}, bf16[256,512]{1,0:T(8,128)(2,1)}) conditional(s32[]{:T(128)} %bitcast.10, () %tuple.16, (s32[]{:T(128)}, f32[1024]{0:T(1024)S(1)}, f32[96,256]{1,0:T(8,128)S(1)}, f32[96,256]{1,0:T(8,128)}, f32[256,1024]{1,0:T(8,128)}, /*index=5*/f32[256,1024]{1,0:T(8,128)}, ...), branch_computations={%region_0.1_spmd, %region_1.4_spmd} | conditional | flops 1621776640 | bytes 78190384 | solution.py:1249
  81.9 23.6 %scan_backward.1 = (f32[256,1024]{1,0:T(8,128)}, f32[96,256]{1,0:T(8,128)}, f32[82,1024]{1,0:T(8,128)}) custom-call(f32[96,256]{1,0:T(8,128)S(1)} %get-tuple-element.64.selected_ref, f32[96,256]{1,0:T(8,128)} %get-tuple-element.65.other_ref, f32[256,1024]{1,0:T(8,128)} %get-tuple-element.66.step_pre_ref, f32[256,1024]{1,0:T(8,128)} %get-tuple-element.67.step_ref, ...), custom_call_target="tpu_custom_call" | custom-call | flops 1 | bytes 1 | tf_op jit(solution)/shard_map/cond/branch_1_fun/scan_backward/pallas_call | solution.py:127
  105.5 1.5 collective-permute-start
  107.1 1.8 constant_dynamic-slice_fusion
  109.6 1.4 collective-permute-start.2
  111.7 4.0 %convolve_grad.1 = (bf16[256,1024]{1,0:T(8,128)(2,1)}, f32[8,1024]{1,0:T(8,128)}, f32[8,1024]{1,0:T(8,128)}, f32[101,1024]{1,0:T(8,128)}) custom-call(f32[96,256]{1,0:T(8,128)} %get-tuple-element.78.select_grad_ref.refs_1_, f32[96,256]{1,0:T(8,128)} %copy-done.34, bf16[96,1024]{1,0:T(8,128)(2,1)S(1)} %copy-done.19, ...), custom_call_target="tpu_custom_call" | custom-call | flops 1 | bytes 1 | tf_op jit(solution)/shard_map/cond/branch_1_fun/convolve_grad/pallas_call | solution.py:127
  115.7 1.4 collective-permute-start.1
  117.1 2.0 collective-permute-done.1.next_ref
  119.9 1.5 patched.1.wait_ref.own_ref
  121.3 1.8 collective-permute-start.5
  123.3 2.1 small_quarters.1
  125.4 2.1 collective-permute-start.6
  127.8 1.1 collective-permute-start.8
  128.9 5.9 %fusion.7 = (f32[256]{0:T(256)S(1)}, f32[1024]{0:T(1024)}, f32[256,1024]{1,0:T(8,128)}) fusion(bf16[256,1024]{1,0:T(8,128)(2,1)S(1)} %copy-done.45, f32[1024]{0:T(1024)S(1)} %copy-done.40, f32[256]{0:T(256)S(1)} %bitcast.44, bf16[1024,2,1024]{2,1,0:T(2,128)(2,1)} %get-tuple-element.203, bf16[1,256,1024]{2,1,0:T(8,128)(2,1)S(1)} %bitcast.36, ...), kind=kOutput, calls=%fused_computation.7 | convolution fusion | flops 1076099840 | bytes 6825984 | tf_op jit(solution)/shard_map/cond/branch_1_fun/cte,dce->td/dot_general | solution.py:1202
  134.7 7.0 %collective-permute-done.7.refs_3_.second_ref = bf16[64,1024]{1,0:T(8,128)(2,1)S(1)} collective-permute-done((bf16[64,1024]{1,0:T(8,128)(2,1)}, bf16[64,1024]{1,0:T(8,128)(2,1)S(1)}, u32[]{:S(2)}, u32[]{:S(2)}) %collective-permute-start.7) | collective-permute-done | bytes 131104 | tf_op jit(solution)/shard_map/cond/branch_1_fun/ppermute | solution.py:33
  141.8 3.4 %collective-permute-done.8.refs_4_.third_ref = bf16[64,1024]{1,0:T(8,128)(2,1)S(1)} collective-permute-done((bf16[64,1024]{1,0:T(8,128)(2,1)}, bf16[64,1024]{1,0:T(8,128)(2,1)S(1)}, u32[]{:S(2)}, u32[]{:S(2)}) %collective-permute-start.8) | collective-permute-done | bytes 131104 | tf_op jit(solution)/shard_map/cond/branch_1_fun/ppermute | solution.py:33
  146.1 2.1 pad_maximum_fusion
  148.2 1.8 fusion.32
  150.0 0.9 slice_select_fusion.1.refs_0_
  150.9 1.5 collective-permute-start.10
  152.9 1.6 collective-permute-done.10
  156.5 3.5 %inner_quarter.1 = (f32[80,1024]{1,0:T(8,128)}, bf16[80,1024]{1,0:T(8,128)(2,1)}, bf16[80,1024]{1,0:T(8,128)(2,1)}, bf16[80,1024]{1,0:T(8,128)(2,1)}) custom-call(s32[1]{0:T(128)} %bitcast.place_ref, bf16[256,1024]{1,0:T(8,128)(2,1)} %patched.1.wait_ref.own_ref, bf16[256,1024]{1,0:T(8,128)(2,1)} %after.7.near_ref, ...), custom_call_target="tpu_custom_call" | custom-call | flops 1 | bytes 1 | tf_op jit(solution)/shard_map/cond/branch_1_fun/inner_quarter/pallas_call | solution.py:938
  160.0 1.5 collective-permute-start.12
  161.5 2.5 %collective-permute-start.13 = (bf16[80,1024]{1,0:T(8,128)(2,1)}, bf16[80,1024]{1,0:T(8,128)(2,1)S(1)}, u32[]{:S(2)}, u32[]{:S(2)}) collective-permute-start(bf16[80,1024]{1,0:T(8,128)(2,1)} %get-tuple-element.101), channel_id=1, source_target_pairs={{0,16},{2,18},{4,20},{6,22},{8,24},{10,26},{12,28},{14,30},{16,0},... | collective-permute-start | bytes 491528 | tf_op jit(solution)/shard_map/cond/branch_1_fun/ppermute | solution.py:33
  165.3 4.1 %collective-permute-done.12 = bf16[80,1024]{1,0:T(8,128)(2,1)S(1)} collective-permute-done((bf16[80,1024]{1,0:T(8,128)(2,1)}, bf16[80,1024]{1,0:T(8,128)(2,1)S(1)}, u32[]{:S(2)}, u32[]{:S(2)}) %collective-permute-start.12) | collective-permute-done | bytes 163872 | tf_op jit(solution)/shard_map/cond/branch_1_fun/ppermute | solution.py:33
  169.4 8.4 %collective-permute-done.13 = bf16[80,1024]{1,0:T(8,128)(2,1)S(1)} collective-permute-done((bf16[80,1024]{1,0:T(8,128)(2,1)}, bf16[80,1024]{1,0:T(8,128)(2,1)S(1)}, u32[]{:S(2)}, u32[]{:S(2)}) %collective-permute-start.13) | collective-permute-done | bytes 163872 | tf_op jit(solution)/shard_map/cond/branch_1_fun/ppermute | solution.py:33
  177.8 3.9 %collective-permute-done.14 = bf16[80,1024]{1,0:T(8,128)(2,1)S(1)} collective-permute-done((bf16[80,1024]{1,0:T(8,128)(2,1)}, bf16[80,1024]{1,0:T(8,128)(2,1)S(1)}, u32[]{:S(2)}, u32[]{:S(2)}) %collective-permute-start.14) | collective-permute-done | bytes 163872 | tf_op jit(solution)/shard_map/cond/branch_1_fun/ppermute | solution.py:33
  181.7 1.1 fusion.18
  182.8 3.5 %collective-permute-start.17 = (bf16[80,1024]{1,0:T(8,128)(2,1)S(1)}, bf16[80,1024]{1,0:T(8,128)(2,1)S(1)}, u32[]{:S(2)}, u32[]{:S(2)}) collective-permute-start(bf16[80,1024]{1,0:T(8,128)(2,1)S(1)} %pad_maximum_fusion.4), channel_id=1, source_target_pairs={{0,8},{2,10},{4,12},{6,14},{8,0},{10,2},{12,4},{14,6},{16,24},{18,... | collective-permute-start | bytes 491528 | tf_op jit(solution)/shard_map/cond/branch_1_fun/ppermute | solution.py:33
  186.9 1.5 collective-permute-start.19
  188.4 1.3 collective-permute-start.16
  189.7 1.4 collective-permute-start.15
  191.1 4.5 %collective-permute-done.17 = bf16[80,1024]{1,0:T(8,128)(2,1)S(1)} collective-permute-done((bf16[80,1024]{1,0:T(8,128)(2,1)S(1)}, bf16[80,1024]{1,0:T(8,128)(2,1)S(1)}, u32[]{:S(2)}, u32[]{:S(2)}) %collective-permute-start.17) | collective-permute-done | bytes 163872 | tf_op jit(solution)/shard_map/cond/branch_1_fun/ppermute | solution.py:33
  195.8 8.9 %collective-permute-done.16 = bf16[80,1024]{1,0:T(8,128)(2,1)S(1)} collective-permute-done((bf16[80,1024]{1,0:T(8,128)(2,1)S(1)}, bf16[80,1024]{1,0:T(8,128)(2,1)S(1)}, u32[]{:S(2)}, u32[]{:S(2)}) %collective-permute-start.16) | collective-permute-done | bytes 163872 | tf_op jit(solution)/shard_map/cond/branch_1_fun/ppermute | solution.py:33
  204.9 1.0 pad_maximum_fusion.1
  205.9 1.1 fusion.15
  207.0 1.4 collective-permute-start.29
  208.4 10.7 %all-reduce.3.cloned.1.call-done = (bf16[1024,1024]{1,0:T(8,128)(2,1)}, bf16[1024,1024]{1,0:T(8,128)(2,1)}) async-done(((bf16[1024,1024]{1,0:T(8,128)(2,1)}, bf16[1024,1024]{1,0:T(8,128)(2,1)}), (bf16[1024,1024]{1,0:T(8,128)(2,1)}, bf16[1024,1024]{1,0:T(8,128)(2,1)})) %all-reduce.3.cloned.1.call-update) | async-done | bytes 4194320 | tf_op jit(solution)/shard_map/psum | solution.py:1158
  219.1 4.1 %convert_element_type.61.rest_0_ = f32[1024,1024]{1,0:T(8,128)} convert(bf16[1024,1024]{1,0:T(8,128)(2,1)} %get-tuple-element.216) | non-fusion elementwise | flops 1048576 | bytes 6291456 | tf_op jit(solution)/shard_map/convert_element_type | solution.py:1256
  224.0 4.6 %joined.2.refs_1_.rest_4_ = f32[1024,2,1024]{2,1,0:T(2,128)} custom-call(s32[1]{0:T(128)} %bitcast.20.place_ref, bf16[1024,1024]{1,0:T(8,128)(2,1)} %get-tuple-element.215.gate_ref, bf16[320,1024]{1,0:T(8,128)(2,1)} %get-tuple-element.172.first_ref.rest_0_, bf16[320,1024]{1,0:T(8,128)(2,1)} %copy-done.8, f32[1024,1024]{1,0:T(8,128)} %convert_element_type.61.rest_0_), custom_call_target="tpu_custom_call" | custom-call | flops 1 | bytes 1 | tf_op jit(solution)/shard_map/joined/pallas_call | solution.py:1003
  229.5 2.3 collective-permute-done.31.second_ref.rest_3_
  232.6 6.2 %joined.3 = (f32[1024,2,1024]{2,1,0:T(2,128)}, f32[64,1024]{1,0:T(8,128)}, f32[16,1024]{1,0:T(8,128)}, f32[1,1024]{1,0:T(1,128)}, f32[1,1024]{1,0:T(1,128)}, /*i...) custom-call(s32[1]{0:T(128)} %bitcast.20.place_ref, ...), custom_call_target="tpu_custom_call", output_to_operand_aliasing={{0}: (8, {})} | custom-call | flops 1 | bytes 1 | tf_op jit(solution)/shard_map/joined/pallas_call | solution.py:1003
  (143 shorter events, 15.9 us)
Async XLA Ops:
  7.2 212.0 %all-reduce.3.cloned.1.call-start = ((), (), s32[]{:S(2)}) async-start(), calls=%async_computation | async-start | bytes 8388608 | tf_op jit(solution)/shard_map/psum | solution.py:1158
  7.2 11.4 %collective-permute-start.20 = (bf16[256,512]{1,0:T(8,128)(2,1)}, bf16[256,512]{1,0:T(8,128)(2,1)S(1)}, u32[]{:S(2)}, u32[]{:S(2)}) collective-permute-start(bf16[256,512]{1,0:T(8,128)(2,1)} %own_ref.1), channel_id=1, source_target_pairs={{0,1},{1,0},{2,3},{3,2},{4,5},{5,4},{6,7},{7,6},{8,9},{9,8},{10,11... | collective-permute-start | bytes 786440 | tf_op jit(solution)/shard_map/ppermute | solution.py:33
  11.6 7.0 %collective-permute-start.22 = (bf16[16,512]{1,0:T(8,128)(2,1)}, bf16[16,512]{1,0:T(8,128)(2,1)S(1)}, u32[]{:S(2)}, u32[]{:S(2)}) collective-permute-start(bf16[16,512]{1,0:T(8,128)(2,1)} %edge_rows.1), channel_id=1, source_target_pairs={{0,3},{1,2},{2,5},{3,4},{4,7},{5,6},{6,9},{7,8},{8,11},{9,10},{10,... | collective-permute-start | bytes 49160 | tf_op jit(solution)/shard_map/ppermute | solution.py:51
  13.0 5.6 %collective-permute-start.21 = (bf16[16,512]{1,0:T(8,128)(2,1)}, bf16[16,512]{1,0:T(8,128)(2,1)S(1)}, u32[]{:S(2)}, u32[]{:S(2)}) collective-permute-start(bf16[16,512]{1,0:T(8,128)(2,1)} %edge_rows.1), channel_id=1, source_target_pairs={{0,2},{2,4},{4,6},{6,8},{8,10},{10,12},{12,14},{14,16},{16,18},{18... | collective-permute-start | bytes 49160 | tf_op jit(solution)/shard_map/ppermute | solution.py:28
  17.0 12.9 %collective-permute-start.24 = (bf16[256,512]{1,0:T(8,128)(2,1)}, bf16[256,512]{1,0:T(8,128)(2,1)S(1)}, u32[]{:S(2)}, u32[]{:S(2)}) collective-permute-start(bf16[256,512]{1,0:T(8,128)(2,1)} %param.27), channel_id=1, source_target_pairs={{0,1},{1,0},{2,3},{3,2},{4,5},{5,4},{6,7},{7,6},{8,9},{9,8},{10,11... | collective-permute-start | bytes 786440 | tf_op jit(solution)/shard_map/ppermute | solution.py:33
  21.8 4.0 %copy-start.18 = (bf16[96,1024]{1,0:T(8,128)(2,1)S(1)}, bf16[96,1024]{1,0:T(8,128)(2,1)}, u32[]{:S(2)}) copy-start(bf16[96,1024]{1,0:T(8,128)(2,1)} %select_ref.1) | copy-start | bytes 589828
  21.8 4.0 %copy-start.36 = (f32[4,1024]{1,0:T(4,128)S(1)}, f32[4,1024]{1,0:T(4,128)}, u32[]{:S(2)}) copy-start(f32[4,1024]{1,0:T(4,128)} %conv_weight_ref.1) | copy-start | bytes 49156
  21.8 8.1 %copy-start.14 = (bf16[256,512]{1,0:T(8,128)(2,1)S(1)}, bf16[256,512]{1,0:T(8,128)(2,1)}, u32[]{:S(2)}) copy-start(bf16[256,512]{1,0:T(8,128)(2,1)} %param.27) | copy-start | bytes 786436
  25.8 4.2 %copy-start = (bf16[1024,1024]{1,0:T(8,128)(2,1)S(1)}, bf16[1024,1024]{1,0:T(8,128)(2,1)}, u32[]{:S(2)}) copy-start(bf16[1024,1024]{1,0:T(8,128)(2,1)} %param.25) | copy-start | bytes 6291460
  28.9 4.6 %collective-permute-start.23 = (f32[96,256]{1,0:T(8,128)S(1)}, f32[96,256]{1,0:T(8,128)S(1)}, u32[]{:S(2)}, u32[]{:S(2)}) collective-permute-start(f32[96,256]{1,0:T(8,128)S(1)} %get-tuple-element.153.selected_ref), channel_id=1, source_target_pairs={{0,1},{1,0},{2,3},{3,2},{4,5},{5,4},{6,7},{7,6},{8,9},{9,8},{10,11... | collective-permute-start | bytes 294920 | tf_op jit(solution)/shard_map/ppermute | solution.py:33
  29.9 13.7 %copy-start.10 = (bf16[256,512]{1,0:T(8,128)(2,1)}, bf16[256,512]{1,0:T(8,128)(2,1)S(1)}, u32[]{:S(2)}) copy-start(bf16[256,512]{1,0:T(8,128)(2,1)S(1)} %get-tuple-element.232) | copy-start | bytes 786436
  29.9 13.7 %copy-start.11 = (bf16[256,512]{1,0:T(8,128)(2,1)}, bf16[256,512]{1,0:T(8,128)(2,1)S(1)}, u32[]{:S(2)}) copy-start(bf16[256,512]{1,0:T(8,128)(2,1)S(1)} %get-tuple-element.233) | copy-start | bytes 786436
  30.0 3.6 %copy-start.13 = (f32[16,1024]{1,0:T(8,128)S(1)}, f32[16,1024]{1,0:T(8,128)}, u32[]{:S(2)}) copy-start(f32[16,1024]{1,0:T(8,128)} %decay_log_ref.7) | copy-start | bytes 196612
  30.0 3.6 %copy-start.20 = (bf16[64,1024]{1,0:T(8,128)(2,1)S(1)}, bf16[64,1024]{1,0:T(8,128)(2,1)}, u32[]{:S(2)}) copy-start(bf16[64,1024]{1,0:T(8,128)(2,1)} %step_weight_ref.1) | copy-start | bytes 393220
  33.6 10.0 %copy-start.17 = (f32[96,256]{1,0:T(8,128)}, f32[96,256]{1,0:T(8,128)S(1)}, u32[]{:S(2)}) copy-start(f32[96,256]{1,0:T(8,128)S(1)} %collective-permute-done.23.other_ref) | copy-start | bytes 294916
  33.6 30.7 %copy-start.38 = (f32[1024]{0:T(1024)S(1)}, f32[1024]{0:T(1024)}, u32[]{:S(2)}) copy-start(f32[1024]{0:T(1024)} %param.24) | copy-start | bytes 12292
  43.6 1.7 collective-permute-start.25
  47.9 6.5 %collective-permute-start.26 = (f32[40,1024]{1,0:T(8,128)}, f32[40,1024]{1,0:T(8,128)S(1)}, u32[]{:S(2)}, u32[]{:S(2)}) collective-permute-start(f32[40,1024]{1,0:T(8,128)} %get-tuple-element.158.own_ref), channel_id=1, source_target_pairs={{0,4},{2,6},{4,0},{6,2},{8,12},{10,14},{12,8},{14,10},{16,20},{18,... | collective-permute-start | bytes 491528 | tf_op jit(solution)/shard_map/ppermute | solution.py:33
  56.8 6.8 %collective-permute-start.27 = (f32[16,1024]{1,0:T(8,128)}, f32[16,1024]{1,0:T(8,128)S(1)}, u32[]{:S(2)}, u32[]{:S(2)}) collective-permute-start(f32[16,1024]{1,0:T(8,128)} %get-tuple-element.161), channel_id=1, source_target_pairs={{0,8},{2,10},{4,12},{6,14},{8,16},{10,18},{12,20},{14,22},{16,24},... | collective-permute-start | bytes 196616 | tf_op jit(solution)/shard_map/ppermute | solution.py:28
  61.4 12.5 %collective-permute-start.28 = (f32[16,1024]{1,0:T(8,128)}, f32[16,1024]{1,0:T(8,128)S(1)}, u32[]{:S(2)}, u32[]{:S(2)}) collective-permute-start(f32[16,1024]{1,0:T(8,128)} %get-tuple-element.163), channel_id=1, source_target_pairs={{8,0},{10,2},{12,4},{14,6},{16,8},{18,10},{20,12},{22,14},{24,16},... | collective-permute-start | bytes 196616 | tf_op jit(solution)/shard_map/ppermute | solution.py:28
  74.6 3.2 %copy-start.5 = (bf16[256,1024]{1,0:T(8,128)(2,1)S(1)}, bf16[256,1024]{1,0:T(8,128)(2,1)}, u32[]{:S(2)}) copy-start(bf16[256,1024]{1,0:T(8,128)(2,1)} %get-tuple-element.165) | copy-start | bytes 1572868
  74.6 3.2 %copy-start.21 = (bf16[256,1024]{1,0:T(8,128)(2,1)S(1)}, bf16[256,1024]{1,0:T(8,128)(2,1)}, u32[]{:S(2)}) copy-start(bf16[256,1024]{1,0:T(8,128)(2,1)} %get-tuple-element.166) | copy-start | bytes 1572868
  81.9 23.6 %copy-start.4 = (bf16[256,1024]{1,0:T(8,128)(2,1)}, bf16[256,1024]{1,0:T(8,128)(2,1)S(1)}, u32[]{:S(2)}) copy-start(bf16[256,1024]{1,0:T(8,128)(2,1)S(1)} %get-tuple-element.105) | copy-start | bytes 1572868 | tf_op jit(solution)/shard_map/cond
  105.5 6.1 %copy-start.16 = (f32[256,1024]{1,0:T(8,128)S(1)}, f32[256,1024]{1,0:T(8,128)}, u32[]{:S(2)}) copy-start(f32[256,1024]{1,0:T(8,128)} %get-tuple-element.81.convolved_ref) | copy-start | bytes 3145732 | tf_op jit(solution)/shard_map/cond
  105.5 6.1 %copy-start.19 = (bf16[96,1024]{1,0:T(8,128)(2,1)S(1)}, bf16[96,1024]{1,0:T(8,128)(2,1)}, u32[]{:S(2)}) copy-start(bf16[96,1024]{1,0:T(8,128)(2,1)} %get-tuple-element.79.select_ref) | copy-start | bytes 589828 | tf_op jit(solution)/shard_map/cond
  105.5 5.5 %collective-permute-start = (f32[96,256]{1,0:T(8,128)}, f32[96,256]{1,0:T(8,128)S(1)}, u32[]{:S(2)}, u32[]{:S(2)}) collective-permute-start(f32[96,256]{1,0:T(8,128)} %get-tuple-element.78.select_grad_ref.refs_1_), channel_id=1, source_target_pairs={{0,1},{1,0},{2,3},{3,2},{4,5},{5,4},{6,7},{7,6},{8,9},{9,8},{10,11... | collective-permute-start | bytes 294920 | tf_op jit(solution)/shard_map/cond/branch_1_fun/ppermute | solution.py:33
  108.9 10.3 %collective-permute-start.4 = (bf16[256,256]{1,0:T(8,128)(2,1)S(1)}, bf16[256,256]{1,0:T(8,128)(2,1)S(1)}, u32[]{:S(2)}, u32[]{:S(2)}) collective-permute-start(bf16[256,256]{1,0:T(8,128)(2,1)S(1)} %get-tuple-element.221), channel_id=1, source_target_pairs={{0,6},{2,4},{4,2},{6,0},{8,14},{10,12},{12,10},{14,8},{16,22},{18,... | collective-permute-start | bytes 393224 | tf_op jit(solution)/shard_map/cond/branch_1_fun/ppermute | solution.py:33
  108.9 10.3 %collective-permute-start.3 = (bf16[256,256]{1,0:T(8,128)(2,1)S(1)}, bf16[256,256]{1,0:T(8,128)(2,1)S(1)}, u32[]{:S(2)}, u32[]{:S(2)}) collective-permute-start(bf16[256,256]{1,0:T(8,128)(2,1)S(1)} %get-tuple-element.222), channel_id=1, source_target_pairs={{0,2},{2,0},{4,6},{6,4},{8,10},{10,8},{12,14},{14,12},{16,18},{18,... | collective-permute-start | bytes 393224 | tf_op jit(solution)/shard_map/cond/branch_1_fun/ppermute | solution.py:33
  109.6 9.6 %collective-permute-start.2 = (bf16[256,256]{1,0:T(8,128)(2,1)S(1)}, bf16[256,256]{1,0:T(8,128)(2,1)S(1)}, u32[]{:S(2)}, u32[]{:S(2)}) collective-permute-start(bf16[256,256]{1,0:T(8,128)(2,1)S(1)} %get-tuple-element.223), channel_id=1, source_target_pairs={{0,4},{2,6},{4,0},{6,2},{8,12},{10,14},{12,8},{14,10},{16,20},{18,... | collective-permute-start | bytes 393224 | tf_op jit(solution)/shard_map/cond/branch_1_fun/ppermute | solution.py:33
  111.7 11.5 %copy-start.33 = (f32[256,1]{1,0:T(8,128)S(1)}, f32[256,1]{1,0:T(8,128)}, u32[]{:S(2)}) copy-start(f32[256,1]{1,0:T(8,128)} %get-tuple-element.205) | copy-start | bytes 3076 | tf_op jit(solution)/shard_map/cond
  115.7 13.2 %copy-start.22 = (bf16[256,1024]{1,0:T(8,128)(2,1)S(1)}, bf16[256,1024]{1,0:T(8,128)(2,1)}, u32[]{:S(2)}) copy-start(bf16[256,1024]{1,0:T(8,128)(2,1)} %get-tuple-element.87) | copy-start | bytes 1572868 | tf_op jit(solution)/shard_map/cond
  115.7 13.2 %copy-start.40 = (f32[1024]{0:T(1024)S(1)}, f32[1024]{0:T(1024)}, u32[]{:S(2)}) copy-start(f32[1024]{0:T(1024)} %get-tuple-element.98) | copy-start | bytes 12292 | tf_op jit(solution)/shard_map/cond
  115.7 13.2 %copy-start.45 = (bf16[256,1024]{1,0:T(8,128)(2,1)S(1)}, bf16[256,1024]{1,0:T(8,128)(2,1)}, u32[]{:S(2)}) copy-start(bf16[256,1024]{1,0:T(8,128)(2,1)} %get-tuple-element.89) | copy-start | bytes 1572868 | tf_op jit(solution)/shard_map/cond
  115.7 3.4 %collective-permute-start.1 = (f32[8,1024]{1,0:T(8,128)}, f32[8,1024]{1,0:T(8,128)S(1)}, u32[]{:S(2)}, u32[]{:S(2)}) collective-permute-start(f32[8,1024]{1,0:T(8,128)} %get-tuple-element.85), channel_id=1, source_target_pairs={{2,0},{4,2},{6,4},{8,6},{10,8},{12,10},{14,12},{16,14},{18,16},{20... | collective-permute-start | bytes 98312 | tf_op jit(solution)/shard_map/cond/branch_1_fun/ppermute | solution.py:28
  121.3 23.9 %collective-permute-start.5 = (bf16[256,1024]{1,0:T(8,128)(2,1)}, bf16[256,1024]{1,0:T(8,128)(2,1)S(1)}, u32[]{:S(2)}, u32[]{:S(2)}) collective-permute-start(bf16[256,1024]{1,0:T(8,128)(2,1)} %patched.1.wait_ref.own_ref), channel_id=1, source_target_pairs={{0,4},{2,6},{4,0},{6,2},{8,12},{10,14},{12,8},{14,10},{16,20},{18,... | collective-permute-start | bytes 1572872 | tf_op jit(solution)/shard_map/cond/branch_1_fun/ppermute | solution.py:33
  125.4 9.4 %collective-permute-start.6 = (bf16[64,1024]{1,0:T(8,128)(2,1)}, bf16[64,1024]{1,0:T(8,128)(2,1)S(1)}, u32[]{:S(2)}, u32[]{:S(2)}) collective-permute-start(bf16[64,1024]{1,0:T(8,128)(2,1)} %get-tuple-element.94), channel_id=1, source_target_pairs={{0,2},{2,0},{4,6},{6,4},{8,10},{10,8},{12,14},{14,12},{16,18},{18,... | collective-permute-start | bytes 393224 | tf_op jit(solution)/shard_map/cond/branch_1_fun/ppermute | solution.py:33
  127.5 14.3 %collective-permute-start.7 = (bf16[64,1024]{1,0:T(8,128)(2,1)}, bf16[64,1024]{1,0:T(8,128)(2,1)S(1)}, u32[]{:S(2)}, u32[]{:S(2)}) collective-permute-start(bf16[64,1024]{1,0:T(8,128)(2,1)} %get-tuple-element.95), channel_id=1, source_target_pairs={{0,4},{2,6},{4,0},{6,2},{8,12},{10,14},{12,8},{14,10},{16,20},{18,... | collective-permute-start | bytes 393224 | tf_op jit(solution)/shard_map/cond/branch_1_fun/ppermute | solution.py:33
  127.8 17.4 %collective-permute-start.8 = (bf16[64,1024]{1,0:T(8,128)(2,1)}, bf16[64,1024]{1,0:T(8,128)(2,1)S(1)}, u32[]{:S(2)}, u32[]{:S(2)}) collective-permute-start(bf16[64,1024]{1,0:T(8,128)(2,1)} %get-tuple-element.96), channel_id=1, source_target_pairs={{0,6},{2,4},{4,2},{6,0},{8,14},{10,12},{12,10},{14,8},{16,22},{18,... | collective-permute-start | bytes 393224 | tf_op jit(solution)/shard_map/cond/branch_1_fun/ppermute | solution.py:33
  128.9 17.2 %copy-start.2 = (bf16[256,1024]{1,0:T(8,128)(2,1)S(1)}, bf16[256,1024]{1,0:T(8,128)(2,1)}, u32[]{:S(2)}) copy-start(bf16[256,1024]{1,0:T(8,128)(2,1)} %patched.1.wait_ref.own_ref) | copy-start | bytes 1572868 | tf_op jit(solution)/shard_map/cond
  134.7 13.4 %copy-start.1 = (bf16[1024,1024]{1,0:T(8,128)(2,1)S(1)}, bf16[1024,1024]{1,0:T(8,128)(2,1)}, u32[]{:S(2)}) copy-start(bf16[1024,1024]{1,0:T(8,128)(2,1)} %get-tuple-element.106) | copy-start | bytes 6291460 | tf_op jit(solution)/shard_map/cond
  134.7 10.5 %copy-start.26 = (bf16[64,1024]{1,0:T(8,128)(2,1)}, bf16[64,1024]{1,0:T(8,128)(2,1)S(1)}, u32[]{:S(2)}) copy-start(bf16[64,1024]{1,0:T(8,128)(2,1)S(1)} %collective-permute-done.6.refs_2_.first_ref) | copy-start | bytes 393220 | tf_op jit(solution)/shard_map/cond
  141.8 3.5 %copy-start.27 = (bf16[64,1024]{1,0:T(8,128)(2,1)}, bf16[64,1024]{1,0:T(8,128)(2,1)S(1)}, u32[]{:S(2)}) copy-start(bf16[64,1024]{1,0:T(8,128)(2,1)S(1)} %collective-permute-done.7.refs_3_.second_ref) | copy-start | bytes 393220 | tf_op jit(solution)/shard_map/cond
  145.2 0.9 copy-start.6
  148.2 7.8 %collective-permute-start.9 = (bf16[512,1024]{1,0:T(8,128)(2,1)}, bf16[512,1024]{1,0:T(8,128)(2,1)}, u32[]{:S(2)}, u32[]{:S(2)}) collective-permute-start(bf16[512,1024]{1,0:T(8,128)(2,1)} %pad_maximum_fusion), channel_id=1, source_target_pairs={{0,2},{2,0},{4,6},{6,4},{8,10},{10,8},{12,14},{14,12},{16,18},{18,... | collective-permute-start | bytes 3145736 | tf_op jit(solution)/shard_map/cond/branch_1_fun/ppermute | solution.py:33
  148.2 2.7 %copy-start.39 = (f32[1024]{0:T(1024)S(1)}, f32[1024]{0:T(1024)}, u32[]{:S(2)}) copy-start(f32[1024]{0:T(1024)} %get-tuple-element.214) | copy-start | bytes 12292 | tf_op jit(solution)/shard_map/cond
  149.9 14.5 %copy-start.7 = (f32[256,1024]{1,0:T(8,128)S(1)}, f32[256,1024]{1,0:T(8,128)}, u32[]{:S(2)}) copy-start(f32[256,1024]{1,0:T(8,128)} %get-tuple-element.231) | copy-start | bytes 3145732 | tf_op jit(solution)/shard_map/cond
  150.9 3.6 %collective-permute-start.10 = (f32[1,1024]{1,0:T(1,128)S(1)}, f32[1,1024]{1,0:T(1,128)S(1)}, u32[]{:S(2)}, u32[]{:S(2)}) collective-permute-start(f32[1,1024]{1,0:T(1,128)S(1)} %bitcast.40), channel_id=1, source_target_pairs={{0,1},{1,0},{2,3},{3,2},{4,5},{5,4},{6,7},{7,6},{8,9},{9,8},{10,11... | collective-permute-start | bytes 12296 | tf_op jit(solution)/shard_map/cond/branch_1_fun/ppermute | solution.py:33
  152.4 3.6 %collective-permute-start.11 = (f32[1,256]{1,0:T(1,128)S(1)}, f32[1,256]{1,0:T(1,128)S(1)}, u32[]{:S(2)}, u32[]{:S(2)}) collective-permute-start(f32[1,256]{1,0:T(1,128)S(1)} %bitcast.50), channel_id=1, source_target_pairs={{0,1},{1,0},{2,3},{3,2},{4,5},{5,4},{6,7},{7,6},{8,9},{9,8},{10,11... | collective-permute-start | bytes 3080 | tf_op jit(solution)/shard_map/cond/branch_1_fun/ppermute | solution.py:33
  160.0 26.3 %copy-start.44 = (f32[1,256]{1,0:T(1,128)S(1)}, f32[1,256]{1,0:T(1,128)}, u32[]{:S(2)}) copy-start(f32[1,256]{1,0:T(1,128)} %copy-done.43) | copy-start | bytes 3076 | tf_op jit(solution)/shard_map/cond
  160.0 9.3 %collective-permute-start.12 = (bf16[80,1024]{1,0:T(8,128)(2,1)}, bf16[80,1024]{1,0:T(8,128)(2,1)S(1)}, u32[]{:S(2)}, u32[]{:S(2)}) collective-permute-start(bf16[80,1024]{1,0:T(8,128)(2,1)} %get-tuple-element.100), channel_id=1, source_target_pairs={{0,8},{2,10},{4,12},{6,14},{8,0},{10,2},{12,4},{14,6},{16,24},{18,... | collective-permute-start | bytes 491528 | tf_op jit(solution)/shard_map/cond/branch_1_fun/ppermute | solution.py:33
  161.5 16.3 %collective-permute-start.13 = (bf16[80,1024]{1,0:T(8,128)(2,1)}, bf16[80,1024]{1,0:T(8,128)(2,1)S(1)}, u32[]{:S(2)}, u32[]{:S(2)}) collective-permute-start(bf16[80,1024]{1,0:T(8,128)(2,1)} %get-tuple-element.101), channel_id=1, source_target_pairs={{0,16},{2,18},{4,20},{6,22},{8,24},{10,26},{12,28},{14,30},{16,0},... | collective-permute-start | bytes 491528 | tf_op jit(solution)/shard_map/cond/branch_1_fun/ppermute | solution.py:33
  164.0 17.6 %collective-permute-start.14 = (bf16[80,1024]{1,0:T(8,128)(2,1)}, bf16[80,1024]{1,0:T(8,128)(2,1)S(1)}, u32[]{:S(2)}, u32[]{:S(2)}) collective-permute-start(bf16[80,1024]{1,0:T(8,128)(2,1)} %get-tuple-element.102), channel_id=1, source_target_pairs={{0,24},{2,26},{4,28},{6,30},{8,16},{10,18},{12,20},{14,22},{16,8},... | collective-permute-start | bytes 491528 | tf_op jit(solution)/shard_map/cond/branch_1_fun/ppermute | solution.py:33
  182.8 12.9 %collective-permute-start.17 = (bf16[80,1024]{1,0:T(8,128)(2,1)S(1)}, bf16[80,1024]{1,0:T(8,128)(2,1)S(1)}, u32[]{:S(2)}, u32[]{:S(2)}) collective-permute-start(bf16[80,1024]{1,0:T(8,128)(2,1)S(1)} %pad_maximum_fusion.4), channel_id=1, source_target_pairs={{0,8},{2,10},{4,12},{6,14},{8,0},{10,2},{12,4},{14,6},{16,24},{18,... | collective-permute-start | bytes 491528 | tf_op jit(solution)/shard_map/cond/branch_1_fun/ppermute | solution.py:33
  186.3 19.7 %copy-start.12 = (bf16[256,512]{1,0:T(8,128)(2,1)S(1)}, bf16[256,512]{1,0:T(8,128)(2,1)}, u32[]{:S(2)}) copy-start(bf16[256,512]{1,0:T(8,128)(2,1)} %get-tuple-element.103) | copy-start | bytes 786436 | tf_op jit(solution)/shard_map/cond
  186.3 19.6 %copy-start.15 = (bf16[256,512]{1,0:T(8,128)(2,1)S(1)}, bf16[256,512]{1,0:T(8,128)(2,1)}, u32[]{:S(2)}) copy-start(bf16[256,512]{1,0:T(8,128)(2,1)} %get-tuple-element.107) | copy-start | bytes 786436 | tf_op jit(solution)/shard_map/cond
  186.3 19.6 %collective-permute-start.18 = (f32[256,512]{1,0:T(8,128)}, f32[256,512]{1,0:T(8,128)S(1)}, u32[]{:S(2)}, u32[]{:S(2)}) collective-permute-start(f32[256,512]{1,0:T(8,128)} %after.8), channel_id=1, source_target_pairs={{0,1},{1,0},{2,3},{3,2},{4,5},{5,4},{6,7},{7,6},{8,9},{9,8},{10,11... | collective-permute-start | bytes 1572872 | tf_op jit(solution)/shard_map/cond/branch_1_fun/ppermute | solution.py:33
  186.9 19.1 %collective-permute-start.19 = (f32[256,512]{1,0:T(8,128)}, f32[256,512]{1,0:T(8,128)S(1)}, u32[]{:S(2)}, u32[]{:S(2)}) collective-permute-start(f32[256,512]{1,0:T(8,128)} %after.9), channel_id=1, source_target_pairs={{0,1},{1,0},{2,3},{3,2},{4,5},{5,4},{6,7},{7,6},{8,9},{9,8},{10,11... | collective-permute-start | bytes 1572872 | tf_op jit(solution)/shard_map/cond/branch_1_fun/ppermute | solution.py:33
  188.4 16.3 %collective-permute-start.16 = (bf16[80,1024]{1,0:T(8,128)(2,1)S(1)}, bf16[80,1024]{1,0:T(8,128)(2,1)S(1)}, u32[]{:S(2)}, u32[]{:S(2)}) collective-permute-start(bf16[80,1024]{1,0:T(8,128)(2,1)S(1)} %pad_maximum_fusion.4), channel_id=1, source_target_pairs={{0,16},{2,18},{4,20},{6,22},{8,24},{10,26},{12,28},{14,30},{16,0},... | collective-permute-start | bytes 491528 | tf_op jit(solution)/shard_map/cond/branch_1_fun/ppermute | solution.py:33
  189.7 15.0 %collective-permute-start.15 = (bf16[80,1024]{1,0:T(8,128)(2,1)S(1)}, bf16[80,1024]{1,0:T(8,128)(2,1)S(1)}, u32[]{:S(2)}, u32[]{:S(2)}) collective-permute-start(bf16[80,1024]{1,0:T(8,128)(2,1)S(1)} %pad_maximum_fusion.4), channel_id=1, source_target_pairs={{0,24},{2,26},{4,28},{6,30},{8,16},{10,18},{12,20},{14,22},{16,8},... | collective-permute-start | bytes 491528 | tf_op jit(solution)/shard_map/cond/branch_1_fun/ppermute | solution.py:33
  207.0 16.2 %collective-permute-start.30 = (bf16[320,1024]{1,0:T(8,128)(2,1)}, bf16[320,1024]{1,0:T(8,128)(2,1)S(1)}, u32[]{:S(2)}, u32[]{:S(2)}) collective-permute-start(bf16[320,1024]{1,0:T(8,128)(2,1)} %get-tuple-element.172.first_ref.rest_0_), channel_id=1, source_target_pairs={{0,2},{2,0},{4,6},{6,4},{8,10},{10,8},{12,14},{14,12},{16,18},{18,... | collective-permute-start | bytes 1966088 | tf_op jit(solution)/shard_map/ppermute | solution.py:33
  207.0 21.6 %collective-permute-start.29 = (bf16[320,1024]{1,0:T(8,128)(2,1)}, bf16[320,1024]{1,0:T(8,128)(2,1)S(1)}, u32[]{:S(2)}, u32[]{:S(2)}) collective-permute-start(bf16[320,1024]{1,0:T(8,128)(2,1)} %get-tuple-element.172.first_ref.rest_0_), channel_id=1, source_target_pairs={{0,4},{2,6},{4,0},{6,2},{8,12},{10,14},{12,8},{14,10},{16,20},{18,... | collective-permute-start | bytes 1966088 | tf_op jit(solution)/shard_map/ppermute | solution.py:33
  228.6 0.8 copy-start.3
  229.5 2.3 collective-permute-start.31
  231.8 0.8 copy-start.9
  (15 other events, 10.0 us)
Sparse Core Ops, SparseCore 0:
  80.0 139.1 all-reduce.2

commit v16 on v15

--- a/solution.py
+++ b/solution.py
@@ -853,8 +853,7 @@
 block_rows, used_rows = 16, 12
 
 
-def small_kernel(place_ref, scan_ref, conv_ref, wait_ref, keep_ref, *rest):
-    *sends_refs, rows, blocks = rest
+def small_kernel(core_ref, scan_ref, conv_ref, wait_ref, keep_ref, send_ref, rows, blocks):
     rows[...] = jnp.zeros(rows.shape, f32)
     rows[: scan_ref.shape[0], :] = scan_ref[...]
     rows[scan_ref.shape[0] : scan_ref.shape[0] + conv_ref.shape[0], :] = conv_ref[...]
@@ -863,32 +862,48 @@
         blocks[n * block_rows : n * block_rows + used_rows, :] = rows[
             n * used_rows : (n + 1) * used_rows, :
         ]
-    quarter = keep_ref.shape[0]
-    for n in range(4):
-        start = pl.multiple_of((place_ref[0] ^ n) * quarter, quarter)
-        block = blocks[pl.ds(start, quarter), :]
-        if n == 0:
-            keep_ref[...] = block
-        else:
-            sends_refs[n - 1][...] = block.astype(bf16)
-
-
-def small_quarters(place, scan_small, conv_small, wait):
+    half = keep_ref.shape[0]
+    mine = pl.ds(pl.multiple_of(core_ref[0] * half, half), half)
+    other = pl.ds(pl.multiple_of((1 - core_ref[0]) * half, half), half)
+    keep_ref[...] = blocks[mine, :]
+    send_ref[...] = blocks[other, :].astype(bf16)
+
+
+def small_halves(core, scan_small, conv_small, wait):
     width = scan_small.shape[1]
     return pl.pallas_call(
         small_kernel,
         in_specs=[pl.BlockSpec(memory_space=pltpu.SMEM)]
         + [pl.BlockSpec(memory_space=pltpu.VMEM)] * 2
         + [pl.BlockSpec(memory_space=pl.ANY)],
-        out_shape=[jax.ShapeDtypeStruct((4 * block_rows, width), f32)]
-        + [jax.ShapeDtypeStruct((4 * block_rows, width), bf16)] * 3,
+        out_shape=[jax.ShapeDtypeStruct((8 * block_rows, width), kind) for kind in (f32, bf16)],
         scratch_shapes=[
             pltpu.VMEM((16 * used_rows, width), f32),
             pltpu.VMEM((16 * block_rows, width), f32),
         ],
         cost_estimate=tiny_cost,
-        name="small_quarters",
-    )(place, scan_small, conv_small, wait)
+        name="small_halves",
+    )(core, scan_small, conv_small, wait)
+
+
+def fold_kernel(upper_ref, keep_ref, arrived_ref, out_ref, send_ref):
+    size = out_ref.shape[0]
+    mine = pl.ds(pl.multiple_of(upper_ref[0] * size, size), size)
+    other = pl.ds(pl.multiple_of((1 - upper_ref[0]) * size, size), size)
+    out_ref[...] = keep_ref[mine, :] + arrived_ref[mine, :].astype(f32)
+    send_ref[...] = (keep_ref[other, :] + arrived_ref[other, :].astype(f32)).astype(bf16)
+
+
+def folded(upper, keep, arrived):
+    rows, width = keep.shape
+    return pl.pallas_call(
+        fold_kernel,
+        in_specs=[pl.BlockSpec(memory_space=pltpu.SMEM)]
+        + [pl.BlockSpec(memory_space=pltpu.VMEM)] * 2,
+        out_shape=[jax.ShapeDtypeStruct((rows // 2, width), kind) for kind in (f32, bf16)],
+        cost_estimate=tiny_cost,
+        name="folded",
+    )(upper, keep, arrived)
 
 
 def quarter_kernel(
@@ -901,9 +916,7 @@
     normed_2,
     normed_3,
     small_ref,
-    first_ref,
-    second_ref,
-    third_ref,
+    arrived_ref,
     *rest,
 ):
     keep_ref, *sends_refs, piece, small = rest[-6:]
@@ -914,9 +927,7 @@
         part = lax.dot_general(left[...], right, contract_first, preferred_element_type=f32)
         total = part if total is None else total + part
     piece[...] = total
-    small[...] = small_ref[...] + sum(
-        ref[...].astype(f32) for ref in (first_ref, second_ref, third_ref)
-    )
+    small[...] = small_ref[...] + arrived_ref[...].astype(f32)
     rows, spare = piece.shape[0] // 4, small.shape[0] // 4
     for n in range(4):
         block = place_ref[0] ^ n
@@ -938,7 +949,7 @@
     return pl.pallas_call(
         quarter_kernel,
         in_specs=[pl.BlockSpec(memory_space=pltpu.SMEM)]
-        + [pl.BlockSpec(memory_space=pltpu.VMEM)] * 11
+        + [pl.BlockSpec(memory_space=pltpu.VMEM)] * 9
         + [pl.BlockSpec(memory_space=pl.ANY)] * len(waits),
         out_shape=[jax.ShapeDtypeStruct((rows, width), f32)]
         + [jax.ShapeDtypeStruct((rows, width), bf16)] * 3,
@@ -949,35 +960,43 @@
     )(place, own, near, far, *normed, *smalls, *waits)
 
 
-def join_kernel(place_ref, gate_ref, first_ref, second_ref, *rest, small_rows):
-    at_end = 2 + len(small_rows) if small_rows else 0
-    out_ref = rest[-1 - at_end]
-    step = pl.program_id(0)
-    rows = out_ref.shape[0] // 2
+def put_quarter(out_ref, gate_ref, inner_ref):
+    rows = out_ref.shape[0] // 4
     out_ref[:, 1, :] = gate_ref[...].astype(f32)
-
-    def put(ref):
-        for n in range(2):
-            at = n * (rows + block_rows)
-            out_ref[n * rows : (n + 1) * rows, 0, :] = ref[at : at + rows, :].astype(f32)
-
-    @pl.when(step < 2)
+    for n in range(4):
+        at = n * (rows + block_rows)
+        out_ref[n * rows : (n + 1) * rows, 0, :] = inner_ref[at : at + rows, :].astype(f32)
+
+
+def first_join_kernel(place_ref, gate_ref, first_ref, second_ref, low_ref, out_ref, wide_ref):
+    wide_ref[...] = low_ref[...].astype(f32)
+
+    @pl.when(pl.program_id(0) == 0)
     def _():
-        put(first_ref)
-
-    @pl.when(step >= 2)
+        put_quarter(out_ref, gate_ref, first_ref)
+
+    @pl.when(pl.program_id(0) == 1)
     def _():
-        put(second_ref)
-
-    if not small_rows:
-        return
-    *row_refs, gain_ref, blocks = rest[-at_end:]
-
-    @pl.when(step == 3)
+        put_quarter(out_ref, gate_ref, second_ref)
+
+
+def last_join_kernel(place_ref, gate_ref, first_ref, second_ref, *rest, small_rows):
+    held = rest[:4]
+    out_ref, *row_refs, gain_ref, blocks = rest[5:]
+
+    @pl.when(pl.program_id(0) == 0)
     def _():
-        for flip, ref in enumerate(rest[:4]):
+        put_quarter(out_ref, gate_ref, first_ref)
+
+    @pl.when(pl.program_id(0) == 1)
+    def _():
+        put_quarter(out_ref, gate_ref, second_ref)
+        rows = out_ref.shape[0] // 4
+        for flip, ref in enumerate(held):
+            number = place_ref[0] ^ flip
+            number = (number & 1) * 2 + number // 2
             for n in range(4):
-                at = ((place_ref[0] ^ flip) * 4 + n) * block_rows
+                at = (number * 4 + n) * block_rows
                 taken = ref[(n + 1) * rows + n * block_rows : (n + 1) * (rows + block_rows), :]
                 blocks[pl.ds(pl.multiple_of(at, block_rows), block_rows), :] = taken.astype(f32)
         for ref, start in zip(row_refs, small_rows):
@@ -989,48 +1008,74 @@
         )
 
 
-def joined(place, flip, gate, first, second, before, waits, held=(), small_rows=(), small_counts=()):
+def joined(kernel, place, flip, gate, first, second, specs, operands, out_specs, out_shape, scratch, aliases):
     depth, width = gate.shape
     quarter = depth // 4
-    block = quarter // 2
-    piece = first.shape[0] // 2
 
     def target(j, place):
-        return 2 * (place[0] ^ (flip + j // 2)) + lax.rem(j, 2)
-
-    vmem = pl.BlockSpec(memory_space=pltpu.VMEM)
-    untouched = [*before, *waits]
+        return place[0] ^ (flip + j)
+
+    whole = pl.BlockSpec(first.shape, lambda j, place: (0, 0))
     return pl.pallas_call(
-        functools.partial(join_kernel, small_rows=small_rows),
+        kernel,
         grid_spec=pltpu.PrefetchScalarGridSpec(
             num_scalar_prefetch=1,
-            grid=(4,),
+            grid=(2,),
             in_specs=[
-                pl.BlockSpec((block, width), lambda j, place: (target(j, place), 0)),
-                pl.BlockSpec((piece, width), lambda j, place: (jnp.minimum(j, 1), 0)),
-                pl.BlockSpec((piece, width), lambda j, place: (jnp.maximum(j - 2, 0), 0)),
+                pl.BlockSpec((quarter, width), lambda j, place: (target(j, place), 0)),
+                whole,
+                whole,
             ]
-            + [vmem] * len(held)
-            + [pl.BlockSpec(memory_space=pl.ANY)] * len(untouched),
-            out_specs=[pl.BlockSpec((block, 2, width), lambda j, place: (target(j, place), 0, 0))]
-            + [pl.BlockSpec((rows, width), lambda j, place: (0, 0)) for rows in small_counts],
-            scratch_shapes=[pltpu.VMEM((16 * block_rows, width), f32)] if small_rows else [],
+            + specs,
+            out_specs=[
+                pl.BlockSpec((quarter, 2, width), lambda j, place: (target(j, place), 0, 0))
+            ]
+            + out_specs,
+            scratch_shapes=scratch,
         ),
-        out_shape=[jax.ShapeDtypeStruct((depth, 2, width), f32)]
-        + [jax.ShapeDtypeStruct((rows, width), f32) for rows in small_counts],
-        input_output_aliases={4 + len(held) + k: k for k in range(len(before))},
+        out_shape=[jax.ShapeDtypeStruct((depth, 2, width), f32)] + out_shape,
+        input_output_aliases=aliases,
         compiler_params=pltpu.CompilerParams(vmem_limit_bytes=vmem_bytes),
         cost_estimate=tiny_cost,
         name="joined",
-    )(place, gate, first, second, *held, *untouched)
+    )(place, gate, first, second, *operands)
+
+
+def joined_first(place, gate, first, second, low):
+    rows, width = low.shape
+    half = pl.BlockSpec((rows // 2, width), lambda j, place: (j, 0))
+    kind = jax.ShapeDtypeStruct((rows, width), f32)
+    return joined(
+        first_join_kernel, place, 0, gate, first, second, [half], [low], [half], [kind], [], {}
+    )
+
+
+def joined_last(place, gate, held, begun, small_rows, small_counts):
+    width = gate.shape[1]
+    whole = pl.BlockSpec(held[0].shape, lambda j, place: (0, 0))
+    return joined(
+        functools.partial(last_join_kernel, small_rows=small_rows),
+        place,
+        2,
+        gate,
+        held[2],
+        held[3],
+        [whole] * 4 + [pl.BlockSpec(memory_space=pl.ANY)],
+        [*held, begun],
+        [pl.BlockSpec((rows, width), lambda j, place: (0, 0)) for rows in small_counts],
+        [jax.ShapeDtypeStruct((rows, width), f32) for rows in small_counts],
+        [pltpu.VMEM((16 * block_rows, width), f32)],
+        {8: 0},
+    )
 
 
 def through(decay, total):
     return jnp.exp(decay * total)
 
 
-def round_kernel(second_ref, decay_log_ref, own_ref, other_ref, passed_ref, new_passed_ref, *ends_refs):
-    count = decay_log_ref.shape[0]
+def round_kernel(second_ref, decay_log_ref, own_ref, other_ref, *rest, first):
+    count, width = decay_log_ref.shape
+    new_passed_ref, *ends_refs = rest if first else rest[1:]
     decay = -jnp.exp(decay_log_ref[...])
     second = second_ref[0] > 0
 
@@ -1049,9 +1094,13 @@
         ends_refs[0][:count, :] = state
         ends_refs[0][count : 2 * count, :] = adjoint
         ends_refs[0][2 * count :, :] = jnp.broadcast_to(early[2] + late[2], (8, decay.shape[1]))
-    before, after = passed_ref[:count], passed_ref[count : 2 * count]
-    before_steps = passed_ref[2 * count : 2 * count + 1]
-    after_steps = passed_ref[2 * count + 1 : 2 * count + 2]
+    if first:
+        before = after = jnp.zeros((count, width), f32)
+        before_steps = after_steps = jnp.zeros((1, width), f32)
+    else:
+        before, after = rest[0][:count], rest[0][count : 2 * count]
+        before_steps = rest[0][2 * count : 2 * count + 1]
+        after_steps = rest[0][2 * count + 1 : 2 * count + 2]
     new_passed_ref[:count, :] = before + jnp.where(second, through(decay, before_steps) * other[0], 0.0)
     new_passed_ref[count : 2 * count, :] = after + jnp.where(
         second, 0.0, through(decay, after_steps) * other[1]
@@ -1063,21 +1112,22 @@
 def carried(ends, decay_log):
     count, width = decay_log.shape
     place = lax.axis_index("wide").astype(jnp.int32)
-    passed = jnp.zeros((2 * count + 8, width), f32)
-    packed = ends
+    state = jax.ShapeDtypeStruct((count, width), f32)
+    passed_kind = jax.ShapeDtypeStruct((2 * count + 8, width), f32)
+    packed, passed = ends, []
     vmem = pl.BlockSpec(memory_space=pltpu.VMEM)
-    for k, kinds in enumerate(([ends], [decay_log, decay_log])):
-        passed, *out = pl.pallas_call(
-            round_kernel,
-            in_specs=[pl.BlockSpec(memory_space=pltpu.SMEM)] + [vmem] * 4,
-            out_shape=[jax.ShapeDtypeStruct(kind.shape, f32) for kind in [passed] + kinds],
+    for k, kinds in enumerate(([jax.ShapeDtypeStruct(ends.shape, f32)], [state, state])):
+        new_passed, *out = pl.pallas_call(
+            functools.partial(round_kernel, first=k == 0),
+            in_specs=[pl.BlockSpec(memory_space=pltpu.SMEM)] + [vmem] * (3 + k),
+            out_shape=[passed_kind] + kinds,
             cost_estimate=tiny_cost,
             name="carry_round",
-        )((place >> k & 1)[None], decay_log, packed, swapped(packed, "wide", 2**k), passed)
-        packed = out[0]
+        )((place >> k & 1)[None], decay_log, packed, swapped(packed, "wide", 2**k), *passed)
+        packed, passed = out[0], [new_passed]
     from_before = passed_along(out[0], "wide", 4)
     from_after = passed_along(out[1], "wide", -4)
-    return passed, from_before, from_after
+    return passed[0], from_before, from_after
 
 
 def local(
@@ -1197,20 +1247,21 @@
         following = passed_along(before, "wide", -1)
         inner_grad = patched(segment_ids, inner_main, last, following, *normed_four)
         near = swapped(inner_grad, "wide", 2)
-        keep, *sends = small_quarters(four_place, scan_small, conv_small, inner_grad)
-        smalls = [keep] + [swapped(sends[n - 1], "wide", n) for n in (1, 2, 3)]
+        keep, send = small_halves(wide_place[None] & 1, scan_small, conv_small, inner_grad)
+        keep, send = folded((wide_place >> 1 & 1)[None], keep, swapped(send, "wide", 1))
+        smalls = [keep, swapped(send, "wide", 2)]
         normed_part = jnp.einsum(
             "cte,dce->td", jnp.stack([inner_grad, gate_grad]), in_weight, preferred_element_type=f32
         )
         gain_part = jnp.sum(normed_part * whole * inverse, axis=0, keepdims=True)
         row_part = jnp.sum(normed_part * norm_gain * whole, axis=1)[None]
-        near = after(near, gain_part, *smalls[1:])
-        far = swapped(jnp.concatenate([inner_grad, near]), "wide", 1)
         first_bits, *more_bits = group_bits(2)
         gain_sum = gain_part + swapped(gain_part, "narrow", 1)
         for bit in (bit for bits in more_bits for bit in bits):
             gain_sum = gain_sum + swapped(gain_sum, "wide", bit)
         row_theirs = swapped(row_part, "narrow", 1)
+        near = after(near, gain_sum, row_theirs, smalls[1])
+        far = swapped(jnp.concatenate([inner_grad, near]), "wide", 1)
         keep, *sends = inner_quarter(
             (wide_place >> 2 & 3)[None],
             inner_grad,
@@ -1218,13 +1269,13 @@
             far,
             normed_four,
             smalls,
-            [gain_sum, row_theirs],
+            [],
         )
         normed_mine, normed_other = narrow_halves(normed_part)
         normed_theirs = swapped(after(normed_other, keep), "narrow", 1)
-        out_part = jnp.dot(gated, out_weight, preferred_element_type=f32)
+        out_part = jnp.dot(after(gated, keep), out_weight, preferred_element_type=f32)
         out_mine, out_other = narrow_halves(out_part)
-        out_theirs = swapped(after(out_other, keep), "narrow", 1)
+        out_theirs = swapped(out_other, "narrow", 1)
         layer_out = (tokens.astype(f32) + (out_mine + out_theirs)).astype(bf16)
         row_sum = (row_part + row_theirs).reshape(rows, 1)
         gain_mine = jnp.where(right_half, norm_gain[features:], norm_gain[:features])
@@ -1247,15 +1298,14 @@
 
     kinds = jax.eval_shape(after_forward, products)
     held, layer_out, tokens_grad = lax.cond(
-        segment_ids[0] >= 0,
+        wide_place >= 0,
         after_forward,
         lambda pair: jax.tree.map(lambda kind: jnp.zeros(kind.shape, kind.dtype), kinds),
         products,
     )
 
-    out_weight_grad = out_sum.astype(f32)
     core = swapped(held, "wide", 1)
-    (begun,) = joined(four_place, 0, gate_sum, held, core, (), (out_weight_grad,))
+    begun, out_weight_grad = joined_first(four_place, gate_sum, held, core, out_sum)
     near = after(swapped(held, "wide", 2), begun)
     far = swapped(near, "wide", 1)
     conv_at = rank + count + 2
@@ -1269,15 +1319,11 @@
         conv_weight_grad,
         conv_bias_grad,
         norm_gain_grad,
-    ) = joined(
+    ) = joined_last(
         four_place,
-        2,
         gate_sum,
-        near,
-        far,
-        (begun,),
-        (),
         (held, core, near, far),
+        begun,
         (0, rank, rank + count, rank + count + 1, conv_at, conv_at + columns, conv_at + columns + taps),
         (rank, count, 1, 1, columns, taps, 1, 1),
     )

time: 247 us -> 236 us (0.955)
  other arithmetic: 12 us -> 6.02 us
  waiting for transfers between devices: 68 us -> 63.3 us
  matrix products: 17.6 us -> 15 us
    convert_element_type x1 -> x0, other arithmetic: 4.07 us -> none  [local(): out_weight_grad = out_sum.astype(f32)]
    ppermute x27 -> x26, waiting for transfers between devices: 54.3 us -> 52.4 us  [swapped(): return lax.ppermute(array, axis, [(i, i ^ bit) for i in range(peers)])]
    pallas_call x5 -> x6, Pallas kernels: 16.6 us -> 18.5 us  [the longest x2 10.8 us: joined(): pl.pallas_call(kernel, grid_spec=pltpu.PrefetchScalarGridSpec(num_scalar_...]
    ppermute x27 -> x26, starting transfers between devices: 32.5 us -> 33.6 us  [swapped(): return lax.ppermute(array, axis, [(i, i ^ bit) for i in range(peers)])]
  transfers between devices with their start and end apart: 33 -> 32, of which waited for: 17 -> 15; matrix products, arithmetic and copies ran while one was open for 11% -> 8% of each run, Pallas kernels for 23% -> 25%
where the time goes in v16:
time: 236 us; the launch traced here: 235 us
  Pallas kernels  77.5 us (33%)
  waiting for transfers between devices  63.3 us (27%)
  starting transfers between devices  46.6 us (20%)
  matrix products  15 us (6%)
  between operations  14.3 us (6%)
  local copies, waits for them, and re-layouts  12 us (5%)
  other arithmetic  6.02 us (3%)
    ppermute x26, waiting for transfers between devices, swapped(): return lax.ppermute(array, axis, [(i, i ^ bit) for i in range(peers)])  52.4 us
    pallas_call x5, Pallas kernels, call(): pl.pallas_call(kernel, grid=(width // scan_width,), in_specs=in_specs, ou...  50.2 us
    ppermute x26, starting transfers between devices, swapped(): return lax.ppermute(array, axis, [(i, i ^ bit) for i in range(peers)])  33.6 us
    ppermute x4, starting transfers between devices, passed_along(): return lax.ppermute(array, axis, pairs)  11.7 us
    pallas_call x2, Pallas kernels, joined(): pl.pallas_call(kernel, grid_spec=pltpu.PrefetchScalarGridSpec(num_scalar_...  10.8 us
    psum x1, waiting for transfers between devices, local(): out_sum, gate_sum = lax.psum(products, 'wide')  9.35 us
    unnamed x44, local copies, waits for them, and re-layouts  5.04 us
  transfers between devices with their start and end apart: 32, of which 15 were waited for; matrix products, arithmetic and copies ran while one was open for 8% of the time, Pallas kernels for 25%

profile of v16, /device:TPU:0, one launch (start us, length us, event | category | flops | bytes accessed | tf_op | source)
XLA Modules:
  0.0 234.9 jit_solution(6785442870847845942)
XLA Ops:
  7.2 3.0 %collective-permute-start.19 = (bf16[256,512]{1,0:T(8,128)(2,1)}, bf16[256,512]{1,0:T(8,128)(2,1)S(1)}, u32[]{:S(2)}, u32[]{:S(2)}) collective-permute-start(bf16[256,512]{1,0:T(8,128)(2,1)} %own_ref.1), channel_id=1, source_target_pairs={{0,1},{1,0},{2,3},{3,2},{4,5},{5,4},{6,7},{7,6},{8,9},{9,8},{10,11... | collective-permute-start | bytes 786440 | tf_op jit(solution)/shard_map/ppermute | solution.py:33
  10.3 1.4 edge_rows.1
  11.6 1.3 collective-permute-start.21
  13.0 4.0 %collective-permute-start.20 = (bf16[16,512]{1,0:T(8,128)(2,1)}, bf16[16,512]{1,0:T(8,128)(2,1)S(1)}, u32[]{:S(2)}, u32[]{:S(2)}) collective-permute-start(bf16[16,512]{1,0:T(8,128)(2,1)} %edge_rows.1), channel_id=1, source_target_pairs={{0,2},{2,4},{4,6},{6,8},{8,10},{10,12},{12,14},{14,16},{16,18},{18... | collective-permute-start | bytes 49160 | tf_op jit(solution)/shard_map/ppermute | solution.py:28
  17.0 1.6 collective-permute-start.23
  19.3 2.5 %normalized.1 = (bf16[256,1024]{1,0:T(8,128)(2,1)}, bf16[272,1024]{1,0:T(8,128)(2,1)}, bf16[256,1024]{1,0:T(8,128)(2,1)}, f32[256,1]{1,0:T(8,128)}, f32[256,128]{1,0:T(8,128)S(1)}) custom-call(bf16[256,512]{1,0:T(8,128)(2,1)} %own_ref.1, bf16[256,512]{1,0:T(8,128)(2,1)} %copy-done.28, bf16[16,512]{1,0:T(8,128)(2,1)} %copy-done.38, ...), custom_call_target="tpu_custom_call" | custom-call | flops 1 | bytes 1 | tf_op jit(solution)/shard_map/normalized/pallas_call | solution.py:768
  21.8 4.0 %fusion.25.inner_ref.gate_ref = bf16[2,272,1024]{2,1,0:T(8,128)(2,1)S(1)} fusion(bf16[1024,2,1024]{2,1,0:T(2,128)(2,1)} %param.17, bf16[272,1024]{1,0:T(8,128)(2,1)} %get-tuple-element.150), kind=kOutput, calls=%fused_computation.49 | convolution fusion | flops 1141407744 | bytes 5865472 | tf_op jit(solution)/shard_map/td,dce->cte/dot_general | solution.py:1167
  25.8 3.1 %convolve.1 = (f32[256,1024]{1,0:T(8,128)}, bf16[256,1024]{1,0:T(8,128)(2,1)S(1)}, f32[96,256]{1,0:T(8,128)S(1)}) custom-call(bf16[2,272,1024]{2,1,0:T(8,128)(2,1)S(1)} %fusion.25.inner_ref.gate_ref, f32[4,1024]{1,0:T(4,128)S(1)} %copy-done.33, f32[1,1024]{1,0:T(1,128)} %bitcast.44, bf16[96,1024]{1,0:T(8,128)(2,1)S(1)} %copy-done.21, ...), custom_call_target="tpu_custom_call" | custom-call | flops 1 | bytes 1 | tf_op jit(solution)/shard_map/convolve/pallas_call | solution.py:127
  28.9 0.9 collective-permute-start.22
  30.7 2.8 %collective-permute-done.22.other_ref = f32[96,256]{1,0:T(8,128)S(1)} collective-permute-done((f32[96,256]{1,0:T(8,128)S(1)}, f32[96,256]{1,0:T(8,128)S(1)}, u32[]{:S(2)}, u32[]{:S(2)}) %collective-permute-start.22) | collective-permute-done | bytes 98336 | tf_op jit(solution)/shard_map/ppermute | solution.py:33
  33.5 9.9 %scan_ends.1 = (f32[256,1024]{1,0:T(8,128)}, f32[256,1024]{1,0:T(8,128)}, f32[40,1024]{1,0:T(8,128)}) custom-call(f32[96,256]{1,0:T(8,128)S(1)} %get-tuple-element.152.selected_ref, f32[96,256]{1,0:T(8,128)S(1)} %collective-permute-done.22.other_ref, bf16[64,1024]{1,0:T(8,128)(2,1)S(1)} %copy-done.23, f32[1,1024]{1,0:T(1,128)} %bitcast.45, ...), custom_call_target="tpu_custom_call" | custom-call | flops 1 | bytes 1 | tf_op jit(solution)/shard_map/scan_ends/pallas_call | solution.py:127
  43.6 1.6 collective-permute-done.24.other_ref
  45.8 1.8 carry_round.2
  47.6 1.7 collective-permute-start.25
  49.3 4.8 %collective-permute-done.25.other_ref = f32[40,1024]{1,0:T(8,128)S(1)} collective-permute-done((f32[40,1024]{1,0:T(8,128)}, f32[40,1024]{1,0:T(8,128)S(1)}, u32[]{:S(2)}, u32[]{:S(2)}) %collective-permute-start.25) | collective-permute-done | bytes 163872 | tf_op jit(solution)/shard_map/ppermute | solution.py:33
  54.7 1.8 carry_round.3
  56.5 4.6 %collective-permute-start.26 = (f32[16,1024]{1,0:T(8,128)}, f32[16,1024]{1,0:T(8,128)S(1)}, u32[]{:S(2)}, u32[]{:S(2)}) collective-permute-start(f32[16,1024]{1,0:T(8,128)} %get-tuple-element.160), channel_id=1, source_target_pairs={{0,8},{2,10},{4,12},{6,14},{8,16},{10,18},{12,20},{14,22},{16,24},... | collective-permute-start | bytes 196616 | tf_op jit(solution)/shard_map/ppermute | solution.py:28
  61.1 1.5 collective-permute-start.27
  64.0 9.7 %scan_forward.1 = (bf16[256,1024]{1,0:T(8,128)(2,1)S(1)}, bf16[256,1024]{1,0:T(8,128)(2,1)}, f32[16,1024]{1,0:T(8,128)}) custom-call(f32[96,256]{1,0:T(8,128)S(1)} %get-tuple-element.152.selected_ref, f32[96,256]{1,0:T(8,128)} %copy-done.20, f32[256,1024]{1,0:T(8,128)} %get-tuple-element.155.step_ref, bf16[256,1024]{1,0:T(8,128)(2,1)S(1)} %get-tuple-element.153.act_ref, ...), custom_call_target="tpu_custom_call" | custom-call | flops 1 | bytes 1 | tf_op jit(solution)/shard_map/scan_forward/pallas_call | solution.py:127
  74.3 3.2 %convolution_convert_fusion = bf16[1024,1024]{1,0:T(8,128)(2,1)} fusion(bf16[256,1024]{1,0:T(8,128)(2,1)S(1)} %after.10, bf16[256,512]{1,0:T(8,128)(2,1)} %copy-done.12, bf16[256,512]{1,0:T(8,128)(2,1)} %copy-done.11), kind=kOutput, calls=%fused_computation.46 | convolution fusion | flops 538968064 | bytes 3145728 | tf_op jit(solution)/shard_map/dot_general | solution.py:1205
  77.4 2.1 convolution_convert_fusion.1
  79.5 122.0 %conditional.1 = (bf16[320,1024]{1,0:T(8,128)(2,1)}, bf16[256,512]{1,0:T(8,128)(2,1)}, bf16[256,512]{1,0:T(8,128)(2,1)}) conditional(s32[]{:T(128)} %convert_element_type.49, () %tuple.16, (s32[]{:T(128)}, f32[1024]{0:T(1024)S(1)}, f32[96,256]{1,0:T(8,128)S(1)}, f32[96,256]{1,0:T(8,128)}, f32[256,1024]{1,0:T(8,128)}, ...), branch_computations={%region_0.1_spmd, %region_1.4_spmd} | conditional | flops 1621776640 | bytes 85772024 | solution.py:1300
  79.5 23.5 %scan_backward.1 = (f32[256,1024]{1,0:T(8,128)}, f32[96,256]{1,0:T(8,128)}, f32[82,1024]{1,0:T(8,128)}) custom-call(f32[96,256]{1,0:T(8,128)S(1)} %get-tuple-element.62.selected_ref, f32[96,256]{1,0:T(8,128)} %get-tuple-element.63.other_ref, f32[256,1024]{1,0:T(8,128)} %get-tuple-element.64.step_pre_ref, f32[256,1024]{1,0:T(8,128)} %get-tuple-element.65.step_ref, ...), custom_call_target="tpu_custom_call" | custom-call | flops 1 | bytes 1 | tf_op jit(solution)/shard_map/cond/branch_1_fun/scan_backward/pallas_call | solution.py:127
  103.1 1.5 collective-permute-start
  104.6 1.9 constant_dynamic-slice_fusion
  107.2 1.4 collective-permute-start.2
  108.7 4.0 %convolve_grad.1 = (bf16[256,1024]{1,0:T(8,128)(2,1)}, f32[8,1024]{1,0:T(8,128)}, f32[8,1024]{1,0:T(8,128)}, f32[101,1024]{1,0:T(8,128)}) custom-call(f32[96,256]{1,0:T(8,128)} %get-tuple-element.76.select_grad_ref.refs_1_, f32[96,256]{1,0:T(8,128)} %collective-permute-done.other_ref, bf16[96,1024]{1,0:T(8,128)(2,1)S(1)} %copy-done.22, ...), custom_call_target="tpu_custom_call" | custom-call | flops 1 | bytes 1 | tf_op jit(solution)/shard_map/cond/branch_1_fun/convolve_grad/pallas_call | solution.py:127
  112.7 1.6 collective-permute-start.1
  114.3 1.0 copy.35
  116.7 1.4 patched.1.wait_ref.own_ref
  118.2 1.9 collective-permute-start.5
  120.0 2.2 small_halves.1
  122.3 2.1 collective-permute-start.8
  124.4 4.3 %fusion.7 = (f32[256]{0:T(256)S(1)}, f32[1024]{0:T(1024)S(1)}, f32[256,1024]{1,0:T(8,128)S(1)}) fusion(bf16[256,1024]{1,0:T(8,128)(2,1)} %get-tuple-element.87, f32[1024]{0:T(1024)S(1)} %copy-done.36, f32[256]{0:T(256)S(1)} %bitcast.42, bf16[1024,2,1024]{2,1,0:T(2,128)(2,1)} %get-tuple-element.204, bf16[1,256,1024]{2,1,0:T(8,128)(2,1)S(1)} %bitcast.37, ...), kind=kOutput, calls=%fused_computation.7 | convolution fusion | flops 1076099840 | bytes 6825984 | tf_op jit(solution)/shard_map/cond/branch_1_fun/cte,dce->td/dot_general | solution.py:1253
  128.7 0.9 collective-permute-start.6
  129.6 1.2 collective-permute-start.7
  131.5 1.9 folded.1
  134.3 5.6 %collective-permute-done.9.refs_3_.arrived_ref = bf16[64,1024]{1,0:T(8,128)(2,1)S(1)} collective-permute-done((bf16[64,1024]{1,0:T(8,128)(2,1)}, bf16[64,1024]{1,0:T(8,128)(2,1)S(1)}, u32[]{:S(2)}, u32[]{:S(2)}) %collective-permute-start.9) | collective-permute-done | bytes 131104 | tf_op jit(solution)/shard_map/cond/branch_1_fun/ppermute | solution.py:33
  140.7 2.1 pad_maximum_fusion
  142.8 0.9 slice_select_fusion.refs_0_
  143.8 1.9 collective-permute-done.10.far_ref
  145.7 1.0 copy-done.16
  146.7 3.5 %inner_quarter.1 = (f32[80,1024]{1,0:T(8,128)}, bf16[80,1024]{1,0:T(8,128)(2,1)}, bf16[80,1024]{1,0:T(8,128)(2,1)}, bf16[80,1024]{1,0:T(8,128)(2,1)}) custom-call(s32[1]{0:T(128)} %bitcast.place_ref, bf16[256,1024]{1,0:T(8,128)(2,1)} %patched.1.wait_ref.own_ref, bf16[256,1024]{1,0:T(8,128)(2,1)} %after.7.near_ref, bf16[512,1024]{1,0:T(8,128)(2,1)} %copy-done.16, ...), custom_call_target="tpu_custom_call" | custom-call | flops 1 | bytes 1 | tf_op jit(solution)/shard_map/cond/branch_1_fun/inner_quarter/pallas_call | solution.py:949
  150.2 0.9 copy-done.43
  151.1 2.4 %collective-permute-start.11 = (bf16[80,1024]{1,0:T(8,128)(2,1)S(1)}, bf16[80,1024]{1,0:T(8,128)(2,1)S(1)}, u32[]{:S(2)}, u32[]{:S(2)}) collective-permute-start(bf16[80,1024]{1,0:T(8,128)(2,1)S(1)} %copy-done.43), channel_id=1, source_target_pairs={{0,8},{2,10},{4,12},{6,14},{8,0},{10,2},{12,4},{14,6},{16,24},{18,... | collective-permute-start | bytes 491528 | tf_op jit(solution)/shard_map/cond/branch_1_fun/ppermute | solution.py:33
  153.5 2.6 %collective-permute-start.12 = (bf16[80,1024]{1,0:T(8,128)(2,1)S(1)}, bf16[80,1024]{1,0:T(8,128)(2,1)S(1)}, u32[]{:S(2)}, u32[]{:S(2)}) collective-permute-start(bf16[80,1024]{1,0:T(8,128)(2,1)S(1)} %copy-done.42), channel_id=1, source_target_pairs={{0,16},{2,18},{4,20},{6,22},{8,24},{10,26},{12,28},{14,30},{16,0},... | collective-permute-start | bytes 491528 | tf_op jit(solution)/shard_map/cond/branch_1_fun/ppermute | solution.py:33
  156.9 7.4 %collective-permute-done.11 = bf16[80,1024]{1,0:T(8,128)(2,1)S(1)} collective-permute-done((bf16[80,1024]{1,0:T(8,128)(2,1)S(1)}, bf16[80,1024]{1,0:T(8,128)(2,1)S(1)}, u32[]{:S(2)}, u32[]{:S(2)}) %collective-permute-start.11) | collective-permute-done | bytes 163872 | tf_op jit(solution)/shard_map/cond/branch_1_fun/ppermute | solution.py:33
  164.2 5.4 %collective-permute-done.12 = bf16[80,1024]{1,0:T(8,128)(2,1)S(1)} collective-permute-done((bf16[80,1024]{1,0:T(8,128)(2,1)S(1)}, bf16[80,1024]{1,0:T(8,128)(2,1)S(1)}, u32[]{:S(2)}, u32[]{:S(2)}) %collective-permute-start.12) | collective-permute-done | bytes 163872 | tf_op jit(solution)/shard_map/cond/branch_1_fun/ppermute | solution.py:33
  169.7 5.5 %collective-permute-start.16 = (bf16[80,1024]{1,0:T(8,128)(2,1)S(1)}, bf16[80,1024]{1,0:T(8,128)(2,1)S(1)}, u32[]{:S(2)}, u32[]{:S(2)}) collective-permute-start(bf16[80,1024]{1,0:T(8,128)(2,1)S(1)} %pad_maximum_fusion.4), channel_id=1, source_target_pairs={{0,8},{2,10},{4,12},{6,14},{8,0},{10,2},{12,4},{14,6},{16,24},{18,... | collective-permute-start | bytes 491528 | tf_op jit(solution)/shard_map/cond/branch_1_fun/ppermute | solution.py:33
  175.3 1.1 collective-permute-start.17
  176.4 1.0 collective-permute-start.18
  177.4 1.1 collective-permute-start.15
  178.5 1.4 collective-permute-start.14
  180.0 5.1 %collective-permute-done.16 = bf16[80,1024]{1,0:T(8,128)(2,1)S(1)} collective-permute-done((bf16[80,1024]{1,0:T(8,128)(2,1)S(1)}, bf16[80,1024]{1,0:T(8,128)(2,1)S(1)}, u32[]{:S(2)}, u32[]{:S(2)}) %collective-permute-start.16) | collective-permute-done | bytes 163872 | tf_op jit(solution)/shard_map/cond/branch_1_fun/ppermute | solution.py:33
  185.2 8.0 %collective-permute-done.15 = bf16[80,1024]{1,0:T(8,128)(2,1)S(1)} collective-permute-done((bf16[80,1024]{1,0:T(8,128)(2,1)S(1)}, bf16[80,1024]{1,0:T(8,128)(2,1)S(1)}, u32[]{:S(2)}, u32[]{:S(2)}) %collective-permute-start.15) | collective-permute-done | bytes 163872 | tf_op jit(solution)/shard_map/cond/branch_1_fun/ppermute | solution.py:33
  193.2 6.2 %collective-permute-done.14 = bf16[80,1024]{1,0:T(8,128)(2,1)S(1)} collective-permute-done((bf16[80,1024]{1,0:T(8,128)(2,1)S(1)}, bf16[80,1024]{1,0:T(8,128)(2,1)S(1)}, u32[]{:S(2)}, u32[]{:S(2)}) %collective-permute-start.14) | collective-permute-done | bytes 163872 | tf_op jit(solution)/shard_map/cond/branch_1_fun/ppermute | solution.py:33
  199.6 0.9 pad_maximum_fusion.1
  200.5 1.0 fusion.15
  201.6 1.0 collective-permute-start.28
  202.6 1.3 collective-permute-done.29.second_ref.rest_1_
  203.9 9.4 %all-reduce.3.cloned.1.call-done = (bf16[1024,1024]{1,0:T(8,128)(2,1)}, bf16[1024,1024]{1,0:T(8,128)(2,1)}) async-done(((bf16[1024,1024]{1,0:T(8,128)(2,1)}, bf16[1024,1024]{1,0:T(8,128)(2,1)}), (bf16[1024,1024]{1,0:T(8,128)(2,1)}, bf16[1024,1024]{1,0:T(8,128)(2,1)})) %all-reduce.3.cloned.1.call-update) | async-done | bytes 4194320 | tf_op jit(solution)/shard_map/psum | solution.py:1208
  213.2 5.6 %joined.2 = (f32[1024,2,1024]{2,1,0:T(2,128)}, f32[1024,1024]{1,0:T(8,128)}) custom-call(s32[1]{0:T(128)} %bitcast.21.place_ref, bf16[1024,1024]{1,0:T(8,128)(2,1)} %get-tuple-element.215.gate_ref, bf16[320,1024]{1,0:T(8,128)(2,1)} %get-tuple-element.171.first_ref.rest_0_, bf16[320,1024]{1,0:T(8,128)(2,1)} %copy-done.10, ...), custom_call_target="tpu_custom_call" | custom-call | flops 1 | bytes 1 | tf_op jit(solution)/shard_map/joined/pallas_call | solution.py:1019
  219.8 2.3 collective-permute-done.30.second_ref.rest_3_
  222.9 5.1 %joined.3 = (f32[1024,2,1024]{2,1,0:T(2,128)}, f32[64,1024]{1,0:T(8,128)}, f32[16,1024]{1,0:T(8,128)}, f32[1,1024]{1,0:T(1,128)}, f32[1,1024]{1,0:T(1,128)}, /*i...) custom-call(s32[1]{0:T(128)} %bitcast.21.place_ref, ...), custom_call_target="tpu_custom_call", output_to_operand_aliasing={{0}: (8, {})} | custom-call | flops 1 | bytes 1 | tf_op jit(solution)/shard_map/joined/pallas_call | solution.py:1019
  (135 shorter events, 12.5 us)
Async XLA Ops:
  7.2 206.1 %all-reduce.3.cloned.1.call-start = ((), (), s32[]{:S(2)}) async-start(), calls=%async_computation | async-start | bytes 8388608 | tf_op jit(solution)/shard_map/psum | solution.py:1208
  7.2 11.4 %collective-permute-start.19 = (bf16[256,512]{1,0:T(8,128)(2,1)}, bf16[256,512]{1,0:T(8,128)(2,1)S(1)}, u32[]{:S(2)}, u32[]{:S(2)}) collective-permute-start(bf16[256,512]{1,0:T(8,128)(2,1)} %own_ref.1), channel_id=1, source_target_pairs={{0,1},{1,0},{2,3},{3,2},{4,5},{5,4},{6,7},{7,6},{8,9},{9,8},{10,11... | collective-permute-start | bytes 786440 | tf_op jit(solution)/shard_map/ppermute | solution.py:33
  11.6 7.0 %collective-permute-start.21 = (bf16[16,512]{1,0:T(8,128)(2,1)}, bf16[16,512]{1,0:T(8,128)(2,1)S(1)}, u32[]{:S(2)}, u32[]{:S(2)}) collective-permute-start(bf16[16,512]{1,0:T(8,128)(2,1)} %edge_rows.1), channel_id=1, source_target_pairs={{0,3},{1,2},{2,5},{3,4},{4,7},{5,6},{6,9},{7,8},{8,11},{9,10},{10,... | collective-permute-start | bytes 49160 | tf_op jit(solution)/shard_map/ppermute | solution.py:51
  13.0 5.6 %collective-permute-start.20 = (bf16[16,512]{1,0:T(8,128)(2,1)}, bf16[16,512]{1,0:T(8,128)(2,1)S(1)}, u32[]{:S(2)}, u32[]{:S(2)}) collective-permute-start(bf16[16,512]{1,0:T(8,128)(2,1)} %edge_rows.1), channel_id=1, source_target_pairs={{0,2},{2,4},{4,6},{6,8},{8,10},{10,12},{12,14},{14,16},{16,18},{18... | collective-permute-start | bytes 49160 | tf_op jit(solution)/shard_map/ppermute | solution.py:28
  17.0 12.9 %collective-permute-start.23 = (bf16[256,512]{1,0:T(8,128)(2,1)}, bf16[256,512]{1,0:T(8,128)(2,1)S(1)}, u32[]{:S(2)}, u32[]{:S(2)}) collective-permute-start(bf16[256,512]{1,0:T(8,128)(2,1)} %param.27), channel_id=1, source_target_pairs={{0,1},{1,0},{2,3},{3,2},{4,5},{5,4},{6,7},{7,6},{8,9},{9,8},{10,11... | collective-permute-start | bytes 786440 | tf_op jit(solution)/shard_map/ppermute | solution.py:33
  21.8 4.0 %copy-start.21 = (bf16[96,1024]{1,0:T(8,128)(2,1)S(1)}, bf16[96,1024]{1,0:T(8,128)(2,1)}, u32[]{:S(2)}) copy-start(bf16[96,1024]{1,0:T(8,128)(2,1)} %select_ref.1) | copy-start | bytes 589828
  21.8 4.0 %copy-start.33 = (f32[4,1024]{1,0:T(4,128)S(1)}, f32[4,1024]{1,0:T(4,128)}, u32[]{:S(2)}) copy-start(f32[4,1024]{1,0:T(4,128)} %conv_weight_ref.1) | copy-start | bytes 49156
  21.8 8.1 %copy-start.17 = (bf16[256,512]{1,0:T(8,128)(2,1)S(1)}, bf16[256,512]{1,0:T(8,128)(2,1)}, u32[]{:S(2)}) copy-start(bf16[256,512]{1,0:T(8,128)(2,1)} %param.27) | copy-start | bytes 786436
  25.8 4.2 %copy-start = (bf16[1024,1024]{1,0:T(8,128)(2,1)S(1)}, bf16[1024,1024]{1,0:T(8,128)(2,1)}, u32[]{:S(2)}) copy-start(bf16[1024,1024]{1,0:T(8,128)(2,1)} %param.25) | copy-start | bytes 6291460
  28.9 4.6 %collective-permute-start.22 = (f32[96,256]{1,0:T(8,128)S(1)}, f32[96,256]{1,0:T(8,128)S(1)}, u32[]{:S(2)}, u32[]{:S(2)}) collective-permute-start(f32[96,256]{1,0:T(8,128)S(1)} %get-tuple-element.152.selected_ref), channel_id=1, source_target_pairs={{0,1},{1,0},{2,3},{3,2},{4,5},{5,4},{6,7},{7,6},{8,9},{9,8},{10,11... | collective-permute-start | bytes 294920 | tf_op jit(solution)/shard_map/ppermute | solution.py:33
  29.9 13.6 %copy-start.11 = (bf16[256,512]{1,0:T(8,128)(2,1)}, bf16[256,512]{1,0:T(8,128)(2,1)S(1)}, u32[]{:S(2)}) copy-start(bf16[256,512]{1,0:T(8,128)(2,1)S(1)} %get-tuple-element.232) | copy-start | bytes 786436
  29.9 13.6 %copy-start.12 = (bf16[256,512]{1,0:T(8,128)(2,1)}, bf16[256,512]{1,0:T(8,128)(2,1)S(1)}, u32[]{:S(2)}) copy-start(bf16[256,512]{1,0:T(8,128)(2,1)S(1)} %get-tuple-element.233) | copy-start | bytes 786436
  29.9 3.6 %copy-start.15 = (f32[16,1024]{1,0:T(8,128)S(1)}, f32[16,1024]{1,0:T(8,128)}, u32[]{:S(2)}) copy-start(f32[16,1024]{1,0:T(8,128)} %decay_log_ref.7) | copy-start | bytes 196612
  29.9 3.6 %copy-start.23 = (bf16[64,1024]{1,0:T(8,128)(2,1)S(1)}, bf16[64,1024]{1,0:T(8,128)(2,1)}, u32[]{:S(2)}) copy-start(bf16[64,1024]{1,0:T(8,128)(2,1)} %step_weight_ref.1) | copy-start | bytes 393220
  33.5 10.0 %copy-start.20 = (f32[96,256]{1,0:T(8,128)}, f32[96,256]{1,0:T(8,128)S(1)}, u32[]{:S(2)}) copy-start(f32[96,256]{1,0:T(8,128)S(1)} %collective-permute-done.22.other_ref) | copy-start | bytes 294916
  33.5 30.4 %copy-start.35 = (f32[1024]{0:T(1024)S(1)}, f32[1024]{0:T(1024)}, u32[]{:S(2)}) copy-start(f32[1024]{0:T(1024)} %param.24) | copy-start | bytes 12292
  43.5 1.7 collective-permute-start.24
  47.6 6.5 %collective-permute-start.25 = (f32[40,1024]{1,0:T(8,128)}, f32[40,1024]{1,0:T(8,128)S(1)}, u32[]{:S(2)}, u32[]{:S(2)}) collective-permute-start(f32[40,1024]{1,0:T(8,128)} %get-tuple-element.157.own_ref), channel_id=1, source_target_pairs={{0,4},{2,6},{4,0},{6,2},{8,12},{10,14},{12,8},{14,10},{16,20},{18,... | collective-permute-start | bytes 491528 | tf_op jit(solution)/shard_map/ppermute | solution.py:33
  56.5 6.8 %collective-permute-start.26 = (f32[16,1024]{1,0:T(8,128)}, f32[16,1024]{1,0:T(8,128)S(1)}, u32[]{:S(2)}, u32[]{:S(2)}) collective-permute-start(f32[16,1024]{1,0:T(8,128)} %get-tuple-element.160), channel_id=1, source_target_pairs={{0,8},{2,10},{4,12},{6,14},{8,16},{10,18},{12,20},{14,22},{16,24},... | collective-permute-start | bytes 196616 | tf_op jit(solution)/shard_map/ppermute | solution.py:28
  61.1 12.5 %collective-permute-start.27 = (f32[16,1024]{1,0:T(8,128)}, f32[16,1024]{1,0:T(8,128)S(1)}, u32[]{:S(2)}, u32[]{:S(2)}) collective-permute-start(f32[16,1024]{1,0:T(8,128)} %get-tuple-element.162), channel_id=1, source_target_pairs={{8,0},{10,2},{12,4},{14,6},{16,8},{18,10},{20,12},{22,14},{24,16},... | collective-permute-start | bytes 196616 | tf_op jit(solution)/shard_map/ppermute | solution.py:28
  74.3 3.2 %copy-start.4 = (bf16[256,1024]{1,0:T(8,128)(2,1)S(1)}, bf16[256,1024]{1,0:T(8,128)(2,1)}, u32[]{:S(2)}) copy-start(bf16[256,1024]{1,0:T(8,128)(2,1)} %get-tuple-element.164) | copy-start | bytes 1572868
  74.3 3.2 %copy-start.24 = (bf16[256,1024]{1,0:T(8,128)(2,1)S(1)}, bf16[256,1024]{1,0:T(8,128)(2,1)}, u32[]{:S(2)}) copy-start(bf16[256,1024]{1,0:T(8,128)(2,1)} %get-tuple-element.165) | copy-start | bytes 1572868
  103.0 5.6 %copy-start.19 = (f32[256,1024]{1,0:T(8,128)S(1)}, f32[256,1024]{1,0:T(8,128)}, u32[]{:S(2)}) copy-start(f32[256,1024]{1,0:T(8,128)} %get-tuple-element.79.convolved_ref) | copy-start | bytes 3145732 | tf_op jit(solution)/shard_map/cond
  103.1 5.6 %copy-start.22 = (bf16[96,1024]{1,0:T(8,128)(2,1)S(1)}, bf16[96,1024]{1,0:T(8,128)(2,1)}, u32[]{:S(2)}) copy-start(bf16[96,1024]{1,0:T(8,128)(2,1)} %get-tuple-element.77.select_ref) | copy-start | bytes 589828 | tf_op jit(solution)/shard_map/cond
  103.1 5.6 %collective-permute-start = (f32[96,256]{1,0:T(8,128)}, f32[96,256]{1,0:T(8,128)}, u32[]{:S(2)}, u32[]{:S(2)}) collective-permute-start(f32[96,256]{1,0:T(8,128)} %get-tuple-element.76.select_grad_ref.refs_1_), channel_id=1, source_target_pairs={{0,1},{1,0},{2,3},{3,2},{4,5},{5,4},{6,7},{7,6},{8,9},{9,8},{10,11... | collective-permute-start | bytes 294920 | tf_op jit(solution)/shard_map/cond/branch_1_fun/ppermute | solution.py:33
  106.5 9.6 %collective-permute-start.4 = (bf16[256,256]{1,0:T(8,128)(2,1)}, bf16[256,256]{1,0:T(8,128)(2,1)}, u32[]{:S(2)}, u32[]{:S(2)}) collective-permute-start(bf16[256,256]{1,0:T(8,128)(2,1)} %get-tuple-element.221), channel_id=1, source_target_pairs={{0,6},{2,4},{4,2},{6,0},{8,14},{10,12},{12,10},{14,8},{16,22},{18,... | collective-permute-start | bytes 393224 | tf_op jit(solution)/shard_map/cond/branch_1_fun/ppermute | solution.py:33
  106.5 9.6 %collective-permute-start.3 = (bf16[256,256]{1,0:T(8,128)(2,1)}, bf16[256,256]{1,0:T(8,128)(2,1)}, u32[]{:S(2)}, u32[]{:S(2)}) collective-permute-start(bf16[256,256]{1,0:T(8,128)(2,1)} %get-tuple-element.222), channel_id=1, source_target_pairs={{0,2},{2,0},{4,6},{6,4},{8,10},{10,8},{12,14},{14,12},{16,18},{18,... | collective-permute-start | bytes 393224 | tf_op jit(solution)/shard_map/cond/branch_1_fun/ppermute | solution.py:33
  107.2 8.9 %collective-permute-start.2 = (bf16[256,256]{1,0:T(8,128)(2,1)}, bf16[256,256]{1,0:T(8,128)(2,1)}, u32[]{:S(2)}, u32[]{:S(2)}) collective-permute-start(bf16[256,256]{1,0:T(8,128)(2,1)} %get-tuple-element.223), channel_id=1, source_target_pairs={{0,4},{2,6},{4,0},{6,2},{8,12},{10,14},{12,8},{14,10},{16,20},{18,... | collective-permute-start | bytes 393224 | tf_op jit(solution)/shard_map/cond/branch_1_fun/ppermute | solution.py:33
  112.7 11.7 %copy-start.25 = (bf16[256,1024]{1,0:T(8,128)(2,1)S(1)}, bf16[256,1024]{1,0:T(8,128)(2,1)}, u32[]{:S(2)}) copy-start(bf16[256,1024]{1,0:T(8,128)(2,1)} %get-tuple-element.85) | copy-start | bytes 1572868 | tf_op jit(solution)/shard_map/cond
  112.7 11.7 %copy-start.36 = (f32[1024]{0:T(1024)S(1)}, f32[1024]{0:T(1024)}, u32[]{:S(2)}) copy-start(f32[1024]{0:T(1024)} %get-tuple-element.89) | copy-start | bytes 12292 | tf_op jit(solution)/shard_map/cond
  112.7 3.4 %collective-permute-start.1 = (f32[8,1024]{1,0:T(8,128)}, f32[8,1024]{1,0:T(8,128)S(1)}, u32[]{:S(2)}, u32[]{:S(2)}) collective-permute-start(f32[8,1024]{1,0:T(8,128)} %get-tuple-element.83), channel_id=1, source_target_pairs={{2,0},{4,2},{6,4},{8,6},{10,8},{12,10},{14,12},{16,14},{18,16},{20... | collective-permute-start | bytes 98312 | tf_op jit(solution)/shard_map/cond/branch_1_fun/ppermute | solution.py:28
  118.2 21.7 %collective-permute-start.5 = (bf16[256,1024]{1,0:T(8,128)(2,1)}, bf16[256,1024]{1,0:T(8,128)(2,1)S(1)}, u32[]{:S(2)}, u32[]{:S(2)}) collective-permute-start(bf16[256,1024]{1,0:T(8,128)(2,1)} %patched.1.wait_ref.own_ref), channel_id=1, source_target_pairs={{0,4},{2,6},{4,0},{6,2},{8,12},{10,14},{12,8},{14,10},{16,20},{18,... | collective-permute-start | bytes 1572872 | tf_op jit(solution)/shard_map/cond/branch_1_fun/ppermute | solution.py:33
  122.3 8.6 %collective-permute-start.8 = (bf16[128,1024]{1,0:T(8,128)(2,1)}, bf16[128,1024]{1,0:T(8,128)(2,1)S(1)}, u32[]{:S(2)}, u32[]{:S(2)}) collective-permute-start(bf16[128,1024]{1,0:T(8,128)(2,1)} %get-tuple-element.93), channel_id=1, source_target_pairs={{0,2},{2,0},{4,6},{6,4},{8,10},{10,8},{12,14},{14,12},{16,18},{18,... | collective-permute-start | bytes 786440 | tf_op jit(solution)/shard_map/cond/branch_1_fun/ppermute | solution.py:33
  128.7 17.0 %copy-start.6 = (f32[256,1024]{1,0:T(8,128)}, f32[256,1024]{1,0:T(8,128)S(1)}, u32[]{:S(2)}) copy-start(f32[256,1024]{1,0:T(8,128)S(1)} %get-tuple-element.231) | copy-start | bytes 3145732 | tf_op jit(solution)/shard_map/cond
  128.7 12.0 %copy-start.2 = (bf16[256,1024]{1,0:T(8,128)(2,1)S(1)}, bf16[256,1024]{1,0:T(8,128)(2,1)}, u32[]{:S(2)}) copy-start(bf16[256,1024]{1,0:T(8,128)(2,1)} %patched.1.wait_ref.own_ref) | copy-start | bytes 1572868 | tf_op jit(solution)/shard_map/cond
  128.7 4.9 %collective-permute-start.6 = (f32[1,1024]{1,0:T(1,128)S(1)}, f32[1,1024]{1,0:T(1,128)S(1)}, u32[]{:S(2)}, u32[]{:S(2)}) collective-permute-start(f32[1,1024]{1,0:T(1,128)S(1)} %bitcast.46), channel_id=1, source_target_pairs={{0,1},{1,0},{2,3},{3,2},{4,5},{5,4},{6,7},{7,6},{8,9},{9,8},{10,11... | collective-permute-start | bytes 12296 | tf_op jit(solution)/shard_map/cond/branch_1_fun/ppermute | solution.py:33
  129.6 4.7 %collective-permute-start.7 = (f32[1,256]{1,0:T(1,128)S(1)}, f32[1,256]{1,0:T(1,128)S(1)}, u32[]{:S(2)}, u32[]{:S(2)}) collective-permute-start(f32[1,256]{1,0:T(1,128)S(1)} %bitcast.50), channel_id=1, source_target_pairs={{0,1},{1,0},{2,3},{3,2},{4,5},{5,4},{6,7},{7,6},{8,9},{9,8},{10,11... | collective-permute-start | bytes 3080 | tf_op jit(solution)/shard_map/cond/branch_1_fun/ppermute | solution.py:33
  133.4 6.4 %collective-permute-start.9 = (bf16[64,1024]{1,0:T(8,128)(2,1)}, bf16[64,1024]{1,0:T(8,128)(2,1)S(1)}, u32[]{:S(2)}, u32[]{:S(2)}) collective-permute-start(bf16[64,1024]{1,0:T(8,128)(2,1)} %get-tuple-element.94), channel_id=1, source_target_pairs={{0,4},{2,6},{4,0},{6,2},{8,12},{10,14},{12,8},{14,10},{16,20},{18,... | collective-permute-start | bytes 393224 | tf_op jit(solution)/shard_map/cond/branch_1_fun/ppermute | solution.py:33
  134.3 5.6 %copy-start.39 = (f32[1,256]{1,0:T(1,128)}, f32[1,256]{1,0:T(1,128)S(1)}, u32[]{:S(2)}) copy-start(f32[1,256]{1,0:T(1,128)S(1)} %collective-permute-done.7.refs_2_) | copy-start | bytes 3076 | tf_op jit(solution)/shard_map/cond
  140.7 3.0 %copy-start.40 = (f32[1,256]{1,0:T(1,128)S(1)}, f32[1,256]{1,0:T(1,128)}, u32[]{:S(2)}) copy-start(f32[1,256]{1,0:T(1,128)} %copy-done.39) | copy-start | bytes 3076 | tf_op jit(solution)/shard_map/cond
  142.8 2.9 %collective-permute-start.10 = (bf16[512,1024]{1,0:T(8,128)(2,1)}, bf16[512,1024]{1,0:T(8,128)(2,1)S(1)}, u32[]{:S(2)}, u32[]{:S(2)}) collective-permute-start(bf16[512,1024]{1,0:T(8,128)(2,1)} %pad_maximum_fusion), channel_id=1, source_target_pairs={{0,2},{2,0},{4,6},{6,4},{8,10},{10,8},{12,14},{14,12},{16,18},{18,... | collective-permute-start | bytes 3145736 | tf_op jit(solution)/shard_map/cond/branch_1_fun/ppermute | solution.py:33
  145.7 1.0 copy-start.16
  150.2 0.9 copy-start.43
  150.2 3.3 %copy-start.42 = (bf16[80,1024]{1,0:T(8,128)(2,1)S(1)}, bf16[80,1024]{1,0:T(8,128)(2,1)}, u32[]{:S(2)}) copy-start(bf16[80,1024]{1,0:T(8,128)(2,1)} %get-tuple-element.98) | copy-start | bytes 491524 | tf_op jit(solution)/shard_map/cond
  150.2 6.0 %copy-start.41 = (bf16[80,1024]{1,0:T(8,128)(2,1)S(1)}, bf16[80,1024]{1,0:T(8,128)(2,1)}, u32[]{:S(2)}) copy-start(bf16[80,1024]{1,0:T(8,128)(2,1)} %get-tuple-element.99) | copy-start | bytes 491524 | tf_op jit(solution)/shard_map/cond
  150.2 6.0 %copy-start.1 = (bf16[1024,1024]{1,0:T(8,128)(2,1)S(1)}, bf16[1024,1024]{1,0:T(8,128)(2,1)}, u32[]{:S(2)}) copy-start(bf16[1024,1024]{1,0:T(8,128)(2,1)} %get-tuple-element.103) | copy-start | bytes 6291460 | tf_op jit(solution)/shard_map/cond
  150.2 19.4 %copy-start.8 = (f32[80,1024]{1,0:T(8,128)S(1)}, f32[80,1024]{1,0:T(8,128)}, u32[]{:S(2)}) copy-start(f32[80,1024]{1,0:T(8,128)} %get-tuple-element.96.refs_1_) | copy-start | bytes 983044 | tf_op jit(solution)/shard_map/cond
  151.1 13.1 %collective-permute-start.11 = (bf16[80,1024]{1,0:T(8,128)(2,1)S(1)}, bf16[80,1024]{1,0:T(8,128)(2,1)S(1)}, u32[]{:S(2)}, u32[]{:S(2)}) collective-permute-start(bf16[80,1024]{1,0:T(8,128)(2,1)S(1)} %copy-done.43), channel_id=1, source_target_pairs={{0,8},{2,10},{4,12},{6,14},{8,0},{10,2},{12,4},{14,6},{16,24},{18,... | collective-permute-start | bytes 491528 | tf_op jit(solution)/shard_map/cond/branch_1_fun/ppermute | solution.py:33
  153.5 16.1 %collective-permute-start.12 = (bf16[80,1024]{1,0:T(8,128)(2,1)S(1)}, bf16[80,1024]{1,0:T(8,128)(2,1)S(1)}, u32[]{:S(2)}, u32[]{:S(2)}) collective-permute-start(bf16[80,1024]{1,0:T(8,128)(2,1)S(1)} %copy-done.42), channel_id=1, source_target_pairs={{0,16},{2,18},{4,20},{6,22},{8,24},{10,26},{12,28},{14,30},{16,0},... | collective-permute-start | bytes 491528 | tf_op jit(solution)/shard_map/cond/branch_1_fun/ppermute | solution.py:33
  156.2 13.4 %collective-permute-start.13 = (bf16[80,1024]{1,0:T(8,128)(2,1)S(1)}, bf16[80,1024]{1,0:T(8,128)(2,1)S(1)}, u32[]{:S(2)}, u32[]{:S(2)}) collective-permute-start(bf16[80,1024]{1,0:T(8,128)(2,1)S(1)} %copy-done.41), channel_id=1, source_target_pairs={{0,24},{2,26},{4,28},{6,30},{8,16},{10,18},{12,20},{14,22},{16,8},... | collective-permute-start | bytes 491528 | tf_op jit(solution)/shard_map/cond/branch_1_fun/ppermute | solution.py:33
  156.9 19.5 %copy-start.14 = (f32[256,512]{1,0:T(8,128)S(1)}, f32[256,512]{1,0:T(8,128)}, u32[]{:S(2)}) copy-start(f32[256,512]{1,0:T(8,128)} %after.9) | copy-start | bytes 1572868 | tf_op jit(solution)/shard_map/cond
  169.7 15.4 %collective-permute-start.16 = (bf16[80,1024]{1,0:T(8,128)(2,1)S(1)}, bf16[80,1024]{1,0:T(8,128)(2,1)S(1)}, u32[]{:S(2)}, u32[]{:S(2)}) collective-permute-start(bf16[80,1024]{1,0:T(8,128)(2,1)S(1)} %pad_maximum_fusion.4), channel_id=1, source_target_pairs={{0,8},{2,10},{4,12},{6,14},{8,0},{10,2},{12,4},{14,6},{16,24},{18,... | collective-permute-start | bytes 491528 | tf_op jit(solution)/shard_map/cond/branch_1_fun/ppermute | solution.py:33
  175.3 25.2 %copy-start.7 = (f32[256,1024]{1,0:T(8,128)S(1)}, f32[256,1024]{1,0:T(8,128)}, u32[]{:S(2)}) copy-start(f32[256,1024]{1,0:T(8,128)} %copy-done.6) | copy-start | bytes 3145732 | tf_op jit(solution)/shard_map/cond
  175.3 25.2 %copy-start.13 = (bf16[256,512]{1,0:T(8,128)(2,1)S(1)}, bf16[256,512]{1,0:T(8,128)(2,1)}, u32[]{:S(2)}) copy-start(bf16[256,512]{1,0:T(8,128)(2,1)} %get-tuple-element.100) | copy-start | bytes 786436 | tf_op jit(solution)/shard_map/cond
  175.3 25.2 %copy-start.18 = (bf16[256,512]{1,0:T(8,128)(2,1)S(1)}, bf16[256,512]{1,0:T(8,128)(2,1)}, u32[]{:S(2)}) copy-start(bf16[256,512]{1,0:T(8,128)(2,1)} %get-tuple-element.104) | copy-start | bytes 786436 | tf_op jit(solution)/shard_map/cond
  175.3 25.2 %collective-permute-start.17 = (f32[256,512]{1,0:T(8,128)S(1)}, f32[256,512]{1,0:T(8,128)S(1)}, u32[]{:S(2)}, u32[]{:S(2)}) collective-permute-start(f32[256,512]{1,0:T(8,128)S(1)} %slice_select_fusion.1), channel_id=1, source_target_pairs={{0,1},{1,0},{2,3},{3,2},{4,5},{5,4},{6,7},{7,6},{8,9},{9,8},{10,11... | collective-permute-start | bytes 1572872 | tf_op jit(solution)/shard_map/cond/branch_1_fun/ppermute | solution.py:33
  176.4 24.1 %collective-permute-start.18 = (f32[256,512]{1,0:T(8,128)S(1)}, f32[256,512]{1,0:T(8,128)S(1)}, u32[]{:S(2)}, u32[]{:S(2)}) collective-permute-start(f32[256,512]{1,0:T(8,128)S(1)} %copy-done.14), channel_id=1, source_target_pairs={{0,1},{1,0},{2,3},{3,2},{4,5},{5,4},{6,7},{7,6},{8,9},{9,8},{10,11... | collective-permute-start | bytes 1572872 | tf_op jit(solution)/shard_map/cond/branch_1_fun/ppermute | solution.py:33
  177.4 15.8 %collective-permute-start.15 = (bf16[80,1024]{1,0:T(8,128)(2,1)S(1)}, bf16[80,1024]{1,0:T(8,128)(2,1)S(1)}, u32[]{:S(2)}, u32[]{:S(2)}) collective-permute-start(bf16[80,1024]{1,0:T(8,128)(2,1)S(1)} %pad_maximum_fusion.4), channel_id=1, source_target_pairs={{0,16},{2,18},{4,20},{6,22},{8,24},{10,26},{12,28},{14,30},{16,0},... | collective-permute-start | bytes 491528 | tf_op jit(solution)/shard_map/cond/branch_1_fun/ppermute | solution.py:33
  178.5 20.9 %collective-permute-start.14 = (bf16[80,1024]{1,0:T(8,128)(2,1)S(1)}, bf16[80,1024]{1,0:T(8,128)(2,1)S(1)}, u32[]{:S(2)}, u32[]{:S(2)}) collective-permute-start(bf16[80,1024]{1,0:T(8,128)(2,1)S(1)} %pad_maximum_fusion.4), channel_id=1, source_target_pairs={{0,24},{2,26},{4,28},{6,30},{8,16},{10,18},{12,20},{14,22},{16,8},... | collective-permute-start | bytes 491528 | tf_op jit(solution)/shard_map/cond/branch_1_fun/ppermute | solution.py:33
  201.6 2.3 collective-permute-start.29
  201.6 17.4 %collective-permute-start.28 = (bf16[320,1024]{1,0:T(8,128)(2,1)}, bf16[320,1024]{1,0:T(8,128)(2,1)S(1)}, u32[]{:S(2)}, u32[]{:S(2)}) collective-permute-start(bf16[320,1024]{1,0:T(8,128)(2,1)} %get-tuple-element.171.first_ref.rest_0_), channel_id=1, source_target_pairs={{0,4},{2,6},{4,0},{6,2},{8,12},{10,14},{12,8},{14,10},{16,20},{18,... | collective-permute-start | bytes 1966088 | tf_op jit(solution)/shard_map/ppermute | solution.py:33
  203.9 9.4 %copy-start.10 = (bf16[320,1024]{1,0:T(8,128)(2,1)}, bf16[320,1024]{1,0:T(8,128)(2,1)S(1)}, u32[]{:S(2)}) copy-start(bf16[320,1024]{1,0:T(8,128)(2,1)S(1)} %collective-permute-done.29.second_ref.rest_1_) | copy-start | bytes 1966084
  219.8 2.3 collective-permute-start.30
  222.1 0.8 copy-start.9
  (12 other events, 8.1 us)
Sparse Core Ops, SparseCore 0:
  79.7 133.5 all-reduce.2

commit v17 on v16

--- a/solution.py
+++ b/solution.py
@@ -1271,18 +1271,8 @@
             smalls,
             [],
         )
-        normed_mine, normed_other = narrow_halves(normed_part)
-        normed_theirs = swapped(after(normed_other, keep), "narrow", 1)
+        row_sum = (row_part + row_theirs).reshape(rows, 1)
         out_part = jnp.dot(after(gated, keep), out_weight, preferred_element_type=f32)
-        out_mine, out_other = narrow_halves(out_part)
-        out_theirs = swapped(out_other, "narrow", 1)
-        layer_out = (tokens.astype(f32) + (out_mine + out_theirs)).astype(bf16)
-        row_sum = (row_part + row_theirs).reshape(rows, 1)
-        gain_mine = jnp.where(right_half, norm_gain[features:], norm_gain[:features])
-        whole_grad = inverse * (gain_mine * (normed_mine + normed_theirs)) - tokens.astype(f32) * (
-            inverse * inverse * inverse
-        ) * (row_sum / (2 * features))
-        tokens_grad = (whole_grad + cotangent.astype(f32)).astype(bf16)
         held = keep
         for n, flip in enumerate(flips(first_bits)[1:]):
             held = held + swapped(sends[n], "wide", flip).astype(f32)
@@ -1294,10 +1284,10 @@
         spare = jnp.broadcast_to(gain_sum, (block_rows - used_rows, gain_sum.shape[1]))
         held = jnp.concatenate([held[: held.shape[0] - spare.shape[0]], spare.astype(bf16)])
         held = gathered(held, first_bits)
-        return held, layer_out, tokens_grad
+        return held, row_sum, *narrow_halves(normed_part), *narrow_halves(out_part)
 
     kinds = jax.eval_shape(after_forward, products)
-    held, layer_out, tokens_grad = lax.cond(
+    held, row_sum, normed_mine, normed_other, out_mine, out_other = lax.cond(
         wide_place >= 0,
         after_forward,
         lambda pair: jax.tree.map(lambda kind: jnp.zeros(kind.shape, kind.dtype), kinds),
@@ -1306,8 +1296,15 @@
 
     core = swapped(held, "wide", 1)
     begun, out_weight_grad = joined_first(four_place, gate_sum, held, core, out_sum)
-    near = after(swapped(held, "wide", 2), begun)
+    near = swapped(held, "wide", 2)
     far = swapped(near, "wide", 1)
+    layer_out = (tokens.astype(f32) + (out_mine + swapped(out_other, "narrow", 1))).astype(bf16)
+    gain_mine = jnp.where(right_half, norm_gain[features:], norm_gain[:features])
+    normed_grad = normed_mine + swapped(normed_other, "narrow", 1)
+    whole_grad = inverse * (gain_mine * normed_grad) - tokens.astype(f32) * (
+        inverse * inverse * inverse
+    ) * (row_sum / (2 * features))
+    tokens_grad = (whole_grad + cotangent.astype(f32)).astype(bf16)
     conv_at = rank + count + 2
     (
         in_weight_grad,

time: 236 us -> 250 us (1.059)
  waiting for transfers between devices: 63.3 us -> 72.4 us
  other arithmetic: 6.02 us -> 11.4 us
    ppermute x26, waiting for transfers between devices: 52.4 us -> 70.9 us  [swapped(): return lax.ppermute(array, axis, [(i, i ^ bit) for i in range(peers)])]
    psum x1, waiting for transfers between devices: 9.35 us -> 0.02 us  [local(): out_sum, gate_sum = lax.psum(products, 'wide')]
  transfers between devices with their start and end apart: 32 -> 32, of which waited for: 15 -> 14; matrix products, arithmetic and copies ran while one was open for 8% -> 10% of each run, Pallas kernels for 25% -> 24%
where the time goes in v17:
time: 250 us; the launch traced here: 249 us
  Pallas kernels  77.8 us (31%)
  waiting for transfers between devices  72.4 us (29%)
  starting transfers between devices  46.6 us (19%)
  matrix products  15 us (6%)
  between operations  14.3 us (6%)
  other arithmetic  11.4 us (5%)
  local copies, waits for them, and re-layouts  11.2 us (4%)
    ppermute x26, waiting for transfers between devices, swapped(): return lax.ppermute(array, axis, [(i, i ^ bit) for i in range(peers)])  70.9 us
    pallas_call x5, Pallas kernels, call(): pl.pallas_call(kernel, grid=(width // scan_width,), in_specs=in_specs, ou...  50.2 us
    ppermute x26, starting transfers between devices, swapped(): return lax.ppermute(array, axis, [(i, i ^ bit) for i in range(peers)])  33.5 us
    ppermute x4, starting transfers between devices, passed_along(): return lax.ppermute(array, axis, pairs)  11.7 us
    pallas_call x2, Pallas kernels, joined(): pl.pallas_call(kernel, grid_spec=pltpu.PrefetchScalarGridSpec(num_scalar_...  10.9 us
    unnamed x44, local copies, waits for them, and re-layouts  5.02 us
  transfers between devices with their start and end apart: 32, of which 14 were waited for; matrix products, arithmetic and copies ran while one was open for 10% of the time, Pallas kernels for 24%

profile of v17, /device:TPU:0, one launch (start us, length us, event | category | flops | bytes accessed | tf_op | source)
XLA Modules:
  0.0 248.8 jit_solution(8828403336956543999)
XLA Ops:
  7.2 3.0 %collective-permute-start.17 = (bf16[256,512]{1,0:T(8,128)(2,1)}, bf16[256,512]{1,0:T(8,128)(2,1)S(1)}, u32[]{:S(2)}, u32[]{:S(2)}) collective-permute-start(bf16[256,512]{1,0:T(8,128)(2,1)} %own_ref.1), channel_id=1, source_target_pairs={{0,1},{1,0},{2,3},{3,2},{4,5},{5,4},{6,7},{7,6},{8,9},{9,8},{10,11... | collective-permute-start | bytes 786440 | tf_op jit(solution)/shard_map/ppermute | solution.py:33
  10.3 1.4 edge_rows.1
  11.6 1.3 collective-permute-start.19
  13.0 4.0 %collective-permute-start.18 = (bf16[16,512]{1,0:T(8,128)(2,1)}, bf16[16,512]{1,0:T(8,128)(2,1)S(1)}, u32[]{:S(2)}, u32[]{:S(2)}) collective-permute-start(bf16[16,512]{1,0:T(8,128)(2,1)} %edge_rows.1), channel_id=1, source_target_pairs={{0,2},{2,4},{4,6},{6,8},{8,10},{10,12},{12,14},{14,16},{16,18},{18... | collective-permute-start | bytes 49160 | tf_op jit(solution)/shard_map/ppermute | solution.py:28
  17.0 1.6 collective-permute-start.21
  19.3 2.5 normalized.1
  21.8 4.0 %fusion.20.inner_ref.gate_ref = bf16[2,272,1024]{2,1,0:T(8,128)(2,1)S(1)} fusion(bf16[1024,2,1024]{2,1,0:T(2,128)(2,1)} %param.17, bf16[272,1024]{1,0:T(8,128)(2,1)} %get-tuple-element.147), kind=kOutput, calls=%fused_computation.42 | convolution fusion | flops 1141407744 | bytes 5865472 | tf_op jit(solution)/shard_map/td,dce->cte/dot_general | solution.py:1167
  25.8 3.1 %convolve.1 = (f32[256,1024]{1,0:T(8,128)}, bf16[256,1024]{1,0:T(8,128)(2,1)S(1)}, f32[96,256]{1,0:T(8,128)S(1)}) custom-call(bf16[2,272,1024]{2,1,0:T(8,128)(2,1)S(1)} %fusion.20.inner_ref.gate_ref, f32[4,1024]{1,0:T(4,128)S(1)} %copy-done.28, f32[1,1024]{1,0:T(1,128)} %bitcast.43, bf16[96,1024]{1,0:T(8,128)(2,1)S(1)} %copy-done.16, ...), custom_call_target="tpu_custom_call" | custom-call | flops 1 | bytes 1 | tf_op jit(solution)/shard_map/convolve/pallas_call | solution.py:127
  28.9 0.9 collective-permute-start.20
  30.7 2.8 %collective-permute-done.20.other_ref = f32[96,256]{1,0:T(8,128)S(1)} collective-permute-done((f32[96,256]{1,0:T(8,128)S(1)}, f32[96,256]{1,0:T(8,128)S(1)}, u32[]{:S(2)}, u32[]{:S(2)}) %collective-permute-start.20) | collective-permute-done | bytes 98336 | tf_op jit(solution)/shard_map/ppermute | solution.py:33
  33.6 10.0 %scan_ends.1 = (f32[256,1024]{1,0:T(8,128)}, f32[256,1024]{1,0:T(8,128)}, f32[40,1024]{1,0:T(8,128)}) custom-call(f32[96,256]{1,0:T(8,128)S(1)} %get-tuple-element.149.selected_ref, f32[96,256]{1,0:T(8,128)S(1)} %collective-permute-done.20.other_ref, bf16[64,1024]{1,0:T(8,128)(2,1)S(1)} %copy-done.18, f32[1,1024]{1,0:T(1,128)} %bitcast.44, ...), custom_call_target="tpu_custom_call" | custom-call | flops 1 | bytes 1 | tf_op jit(solution)/shard_map/scan_ends/pallas_call | solution.py:127
  43.7 1.6 collective-permute-done.22.other_ref
  45.9 1.8 carry_round.2
  47.7 1.7 collective-permute-start.23
  49.4 4.8 %collective-permute-done.23.other_ref = f32[40,1024]{1,0:T(8,128)S(1)} collective-permute-done((f32[40,1024]{1,0:T(8,128)}, f32[40,1024]{1,0:T(8,128)S(1)}, u32[]{:S(2)}, u32[]{:S(2)}) %collective-permute-start.23) | collective-permute-done | bytes 163872 | tf_op jit(solution)/shard_map/ppermute | solution.py:33
  54.8 1.8 carry_round.3
  56.6 4.6 %collective-permute-start.24 = (f32[16,1024]{1,0:T(8,128)}, f32[16,1024]{1,0:T(8,128)S(1)}, u32[]{:S(2)}, u32[]{:S(2)}) collective-permute-start(f32[16,1024]{1,0:T(8,128)} %get-tuple-element.157), channel_id=1, source_target_pairs={{0,8},{2,10},{4,12},{6,14},{8,16},{10,18},{12,20},{14,22},{16,24},... | collective-permute-start | bytes 196616 | tf_op jit(solution)/shard_map/ppermute | solution.py:28
  61.2 1.5 collective-permute-start.25
  64.1 9.7 %scan_forward.1 = (bf16[256,1024]{1,0:T(8,128)(2,1)S(1)}, bf16[256,1024]{1,0:T(8,128)(2,1)}, f32[16,1024]{1,0:T(8,128)}) custom-call(f32[96,256]{1,0:T(8,128)S(1)} %get-tuple-element.149.selected_ref, f32[96,256]{1,0:T(8,128)} %copy-done.15, f32[256,1024]{1,0:T(8,128)} %get-tuple-element.152.step_ref, bf16[256,1024]{1,0:T(8,128)(2,1)S(1)} %get-tuple-element.150.act_ref, ...), custom_call_target="tpu_custom_call" | custom-call | flops 1 | bytes 1 | tf_op jit(solution)/shard_map/scan_forward/pallas_call | solution.py:127
  74.4 3.2 %convolution_convert_fusion = bf16[1024,1024]{1,0:T(8,128)(2,1)} fusion(bf16[256,1024]{1,0:T(8,128)(2,1)S(1)} %after.7, bf16[256,512]{1,0:T(8,128)(2,1)} %copy-done.9, bf16[256,512]{1,0:T(8,128)(2,1)} %copy-done.8), kind=kOutput, calls=%fused_computation.39 | convolution fusion | flops 538968064 | bytes 3145728 | tf_op jit(solution)/shard_map/dot_general | solution.py:1205
  77.5 2.1 convolution_convert_fusion.1
  79.6 120.5 %conditional.1 = (bf16[320,1024]{1,0:T(8,128)(2,1)}, f32[256,1]{0,1:T(1,128)}, f32[256,512]{1,0:T(8,128)}, f32[256,512]{1,0:T(8,128)}, f32[256,512]{1,0:T(8,128)S(1)}, /*index=5*/f32[256,512]{1,0:T(8,128)}) conditional(s32[]{:T(128)} %convert_element_type.50, () %tuple.16, (s32[]{:T(128)}, f32[1024]{0:T(1024)S(1)}, f32[96,256]{1,0:T(8,128)S(1)}, ...), branch_computations={%region_0.1_spmd, %region_1.4_spmd} | conditional | flops 1620071424 | bytes 63869408 | solution.py:1290
  79.6 23.5 %scan_backward.1 = (f32[256,1024]{1,0:T(8,128)}, f32[96,256]{1,0:T(8,128)}, f32[82,1024]{1,0:T(8,128)}) custom-call(f32[96,256]{1,0:T(8,128)S(1)} %get-tuple-element.58.selected_ref, f32[96,256]{1,0:T(8,128)} %get-tuple-element.59.other_ref, f32[256,1024]{1,0:T(8,128)} %get-tuple-element.60.step_pre_ref, f32[256,1024]{1,0:T(8,128)} %get-tuple-element.61.step_ref, ...), custom_call_target="tpu_custom_call" | custom-call | flops 1 | bytes 1 | tf_op jit(solution)/shard_map/cond/branch_1_fun/scan_backward/pallas_call | solution.py:127
  103.1 1.5 collective-permute-start
  104.7 1.9 constant_dynamic-slice_fusion
  107.3 1.4 collective-permute-start.2
  108.7 4.0 %convolve_grad.1 = (bf16[256,1024]{1,0:T(8,128)(2,1)}, f32[8,1024]{1,0:T(8,128)}, f32[8,1024]{1,0:T(8,128)}, f32[101,1024]{1,0:T(8,128)}) custom-call(f32[96,256]{1,0:T(8,128)} %get-tuple-element.72.select_grad_ref.refs_1_, f32[96,256]{1,0:T(8,128)} %collective-permute-done.other_ref, bf16[96,1024]{1,0:T(8,128)(2,1)S(1)} %copy-done.17, ...), custom_call_target="tpu_custom_call" | custom-call | flops 1 | bytes 1 | tf_op jit(solution)/shard_map/cond/branch_1_fun/convolve_grad/pallas_call | solution.py:127
  112.7 1.6 collective-permute-start.1
  114.4 1.0 copy.36
  116.8 1.5 patched.1.wait_ref.own_ref
  118.2 1.9 collective-permute-start.5
  120.1 2.2 small_halves.1
  122.3 2.1 collective-permute-start.8
  124.4 4.3 %fusion.7 = (f32[256]{0:T(256)S(1)}, f32[1024]{0:T(1024)S(1)}, f32[256,1024]{1,0:T(8,128)S(1)}) fusion(bf16[256,1024]{1,0:T(8,128)(2,1)} %get-tuple-element.83, f32[1024]{0:T(1024)S(1)} %copy-done.31, f32[256]{0:T(256)S(1)} %bitcast.48, bf16[1024,2,1024]{2,1,0:T(2,128)(2,1)} %get-tuple-element.232, bf16[1,256,1024]{2,1,0:T(8,128)(2,1)S(1)} %bitcast.38, ...), kind=kOutput, calls=%fused_computation.7 | convolution fusion | flops 1076099840 | bytes 6825984 | tf_op jit(solution)/shard_map/cond/branch_1_fun/cte,dce->td/dot_general | solution.py:1253
  128.8 0.9 collective-permute-start.6
  129.7 1.2 collective-permute-start.7
  131.6 1.9 folded.1
  134.4 5.6 %collective-permute-done.9.refs_3_.arrived_ref = bf16[64,1024]{1,0:T(8,128)(2,1)S(1)} collective-permute-done((bf16[64,1024]{1,0:T(8,128)(2,1)}, bf16[64,1024]{1,0:T(8,128)(2,1)S(1)}, u32[]{:S(2)}, u32[]{:S(2)}) %collective-permute-start.9) | collective-permute-done | bytes 131104 | tf_op jit(solution)/shard_map/cond/branch_1_fun/ppermute | solution.py:33
  140.8 2.2 pad_maximum_fusion
  143.0 1.1 slice_select_fusion.2
  144.7 1.1 collective-permute-done.10.far_ref
  145.9 1.1 copy-done.12
  146.9 3.6 %inner_quarter.1 = (f32[80,1024]{1,0:T(8,128)}, bf16[80,1024]{1,0:T(8,128)(2,1)}, bf16[80,1024]{1,0:T(8,128)(2,1)}, bf16[80,1024]{1,0:T(8,128)(2,1)}) custom-call(s32[1]{0:T(128)} %bitcast.place_ref, bf16[256,1024]{1,0:T(8,128)(2,1)} %patched.1.wait_ref.own_ref, bf16[256,1024]{1,0:T(8,128)(2,1)} %after.5.near_ref, bf16[512,1024]{1,0:T(8,128)(2,1)} %copy-done.12, ...), custom_call_target="tpu_custom_call" | custom-call | flops 1 | bytes 1 | tf_op jit(solution)/shard_map/cond/branch_1_fun/inner_quarter/pallas_call | solution.py:949
  150.6 2.4 collective-permute-start.11
  153.0 2.6 %collective-permute-start.12 = (bf16[80,1024]{1,0:T(8,128)(2,1)}, bf16[80,1024]{1,0:T(8,128)(2,1)S(1)}, u32[]{:S(2)}, u32[]{:S(2)}) collective-permute-start(bf16[80,1024]{1,0:T(8,128)(2,1)} %get-tuple-element.94), channel_id=1, source_target_pairs={{0,16},{2,18},{4,20},{6,22},{8,24},{10,26},{12,28},{14,30},{16,0},... | collective-permute-start | bytes 491528 | tf_op jit(solution)/shard_map/cond/branch_1_fun/ppermute | solution.py:33
  156.3 7.8 %collective-permute-done.11 = bf16[80,1024]{1,0:T(8,128)(2,1)S(1)} collective-permute-done((bf16[80,1024]{1,0:T(8,128)(2,1)}, bf16[80,1024]{1,0:T(8,128)(2,1)S(1)}, u32[]{:S(2)}, u32[]{:S(2)}) %collective-permute-start.11) | collective-permute-done | bytes 163872 | tf_op jit(solution)/shard_map/cond/branch_1_fun/ppermute | solution.py:33
  164.1 5.4 %collective-permute-done.12 = bf16[80,1024]{1,0:T(8,128)(2,1)S(1)} collective-permute-done((bf16[80,1024]{1,0:T(8,128)(2,1)}, bf16[80,1024]{1,0:T(8,128)(2,1)S(1)}, u32[]{:S(2)}, u32[]{:S(2)}) %collective-permute-start.12) | collective-permute-done | bytes 163872 | tf_op jit(solution)/shard_map/cond/branch_1_fun/ppermute | solution.py:33
  169.6 5.4 %collective-permute-start.16 = (bf16[80,1024]{1,0:T(8,128)(2,1)S(1)}, bf16[80,1024]{1,0:T(8,128)(2,1)S(1)}, u32[]{:S(2)}, u32[]{:S(2)}) collective-permute-start(bf16[80,1024]{1,0:T(8,128)(2,1)S(1)} %pad_maximum_fusion.4), channel_id=1, source_target_pairs={{0,8},{2,10},{4,12},{6,14},{8,0},{10,2},{12,4},{14,6},{16,24},{18,... | collective-permute-start | bytes 491528 | tf_op jit(solution)/shard_map/cond/branch_1_fun/ppermute | solution.py:33
  175.0 0.9 slice_select_fusion
  175.9 1.0 collective-permute-start.15
  177.0 1.4 collective-permute-start.14
  178.4 6.9 %collective-permute-done.16 = bf16[80,1024]{1,0:T(8,128)(2,1)S(1)} collective-permute-done((bf16[80,1024]{1,0:T(8,128)(2,1)S(1)}, bf16[80,1024]{1,0:T(8,128)(2,1)S(1)}, u32[]{:S(2)}, u32[]{:S(2)}) %collective-permute-start.16) | collective-permute-done | bytes 163872 | tf_op jit(solution)/shard_map/cond/branch_1_fun/ppermute | solution.py:33
  185.3 5.5 %collective-permute-done.15 = bf16[80,1024]{1,0:T(8,128)(2,1)S(1)} collective-permute-done((bf16[80,1024]{1,0:T(8,128)(2,1)S(1)}, bf16[80,1024]{1,0:T(8,128)(2,1)S(1)}, u32[]{:S(2)}, u32[]{:S(2)}) %collective-permute-start.15) | collective-permute-done | bytes 163872 | tf_op jit(solution)/shard_map/cond/branch_1_fun/ppermute | solution.py:33
  190.8 8.1 %collective-permute-done.14 = bf16[80,1024]{1,0:T(8,128)(2,1)S(1)} collective-permute-done((bf16[80,1024]{1,0:T(8,128)(2,1)S(1)}, bf16[80,1024]{1,0:T(8,128)(2,1)S(1)}, u32[]{:S(2)}, u32[]{:S(2)}) %collective-permute-start.14) | collective-permute-done | bytes 163872 | tf_op jit(solution)/shard_map/cond/branch_1_fun/ppermute | solution.py:33
  199.2 1.0 pad_maximum_fusion.1
  200.1 1.2 collective-permute-start.28
  202.0 1.4 collective-permute-start.27
  203.4 11.0 %collective-permute-done.28.first_ref.rest_2_ = bf16[320,1024]{1,0:T(8,128)(2,1)S(1)} collective-permute-done((bf16[320,1024]{1,0:T(8,128)(2,1)}, bf16[320,1024]{1,0:T(8,128)(2,1)S(1)}, u32[]{:S(2)}, u32[]{:S(2)}) %collective-permute-start.28) | collective-permute-done | bytes 655392 | tf_op jit(solution)/shard_map/ppermute | solution.py:33
  215.2 1.0 fusion.33
  216.9 10.2 %collective-permute-done.27 = f32[256,512]{1,0:T(8,128)S(1)} collective-permute-done((f32[256,512]{1,0:T(8,128)}, f32[256,512]{1,0:T(8,128)S(1)}, u32[]{:S(2)}, u32[]{:S(2)}) %collective-permute-start.27) | collective-permute-done | bytes 524320 | tf_op jit(solution)/shard_map/ppermute | solution.py:33
  227.2 2.2 fusion.28
  230.2 5.6 %joined.2 = (f32[1024,2,1024]{2,1,0:T(2,128)}, f32[1024,1024]{1,0:T(8,128)}) custom-call(s32[1]{0:T(128)} %bitcast.21.place_ref, bf16[1024,1024]{1,0:T(8,128)(2,1)} %get-tuple-element.243.gate_ref, bf16[320,1024]{1,0:T(8,128)(2,1)} %get-tuple-element.171.first_ref.rest_0_, bf16[320,1024]{1,0:T(8,128)(2,1)} %copy-done.7, ...), custom_call_target="tpu_custom_call" | custom-call | flops 1 | bytes 1 | tf_op jit(solution)/shard_map/joined/pallas_call | solution.py:1019
  235.9 0.8 copy-done.6
  236.7 5.2 %joined.3 = (f32[1024,2,1024]{2,1,0:T(2,128)}, f32[64,1024]{1,0:T(8,128)}, f32[16,1024]{1,0:T(8,128)}, f32[1,1024]{1,0:T(1,128)}, f32[1,1024]{1,0:T(1,128)}, /*i...) custom-call(s32[1]{0:T(128)} %bitcast.21.place_ref, ...), custom_call_target="tpu_custom_call", output_to_operand_aliasing={{0}: (8, {})} | custom-call | flops 1 | bytes 1 | tf_op jit(solution)/shard_map/joined/pallas_call | solution.py:1019
  (118 shorter events, 14.2 us)
Async XLA Ops:
  7.2 222.2 %all-reduce.3.cloned.1.call-start = ((), (), s32[]{:S(2)}) async-start(), calls=%async_computation | async-start | bytes 8388608 | tf_op jit(solution)/shard_map/psum | solution.py:1208
  7.2 11.4 %collective-permute-start.17 = (bf16[256,512]{1,0:T(8,128)(2,1)}, bf16[256,512]{1,0:T(8,128)(2,1)S(1)}, u32[]{:S(2)}, u32[]{:S(2)}) collective-permute-start(bf16[256,512]{1,0:T(8,128)(2,1)} %own_ref.1), channel_id=1, source_target_pairs={{0,1},{1,0},{2,3},{3,2},{4,5},{5,4},{6,7},{7,6},{8,9},{9,8},{10,11... | collective-permute-start | bytes 786440 | tf_op jit(solution)/shard_map/ppermute | solution.py:33
  11.6 7.0 %collective-permute-start.19 = (bf16[16,512]{1,0:T(8,128)(2,1)}, bf16[16,512]{1,0:T(8,128)(2,1)S(1)}, u32[]{:S(2)}, u32[]{:S(2)}) collective-permute-start(bf16[16,512]{1,0:T(8,128)(2,1)} %edge_rows.1), channel_id=1, source_target_pairs={{0,3},{1,2},{2,5},{3,4},{4,7},{5,6},{6,9},{7,8},{8,11},{9,10},{10,... | collective-permute-start | bytes 49160 | tf_op jit(solution)/shard_map/ppermute | solution.py:51
  13.0 5.6 %collective-permute-start.18 = (bf16[16,512]{1,0:T(8,128)(2,1)}, bf16[16,512]{1,0:T(8,128)(2,1)S(1)}, u32[]{:S(2)}, u32[]{:S(2)}) collective-permute-start(bf16[16,512]{1,0:T(8,128)(2,1)} %edge_rows.1), channel_id=1, source_target_pairs={{0,2},{2,4},{4,6},{6,8},{8,10},{10,12},{12,14},{14,16},{16,18},{18... | collective-permute-start | bytes 49160 | tf_op jit(solution)/shard_map/ppermute | solution.py:28
  17.0 12.9 %collective-permute-start.21 = (bf16[256,512]{1,0:T(8,128)(2,1)}, bf16[256,512]{1,0:T(8,128)(2,1)S(1)}, u32[]{:S(2)}, u32[]{:S(2)}) collective-permute-start(bf16[256,512]{1,0:T(8,128)(2,1)} %param.27), channel_id=1, source_target_pairs={{0,1},{1,0},{2,3},{3,2},{4,5},{5,4},{6,7},{7,6},{8,9},{9,8},{10,11... | collective-permute-start | bytes 786440 | tf_op jit(solution)/shard_map/ppermute | solution.py:33
  18.6 0.7 copy-start.23
  21.8 4.0 %copy-start.16 = (bf16[96,1024]{1,0:T(8,128)(2,1)S(1)}, bf16[96,1024]{1,0:T(8,128)(2,1)}, u32[]{:S(2)}) copy-start(bf16[96,1024]{1,0:T(8,128)(2,1)} %select_ref.1) | copy-start | bytes 589828
  21.8 4.0 %copy-start.28 = (f32[4,1024]{1,0:T(4,128)S(1)}, f32[4,1024]{1,0:T(4,128)}, u32[]{:S(2)}) copy-start(f32[4,1024]{1,0:T(4,128)} %conv_weight_ref.1) | copy-start | bytes 49156
  21.8 8.1 %copy-start.13 = (bf16[256,512]{1,0:T(8,128)(2,1)S(1)}, bf16[256,512]{1,0:T(8,128)(2,1)}, u32[]{:S(2)}) copy-start(bf16[256,512]{1,0:T(8,128)(2,1)} %param.27) | copy-start | bytes 786436
  25.8 4.2 %copy-start = (bf16[1024,1024]{1,0:T(8,128)(2,1)S(1)}, bf16[1024,1024]{1,0:T(8,128)(2,1)}, u32[]{:S(2)}) copy-start(bf16[1024,1024]{1,0:T(8,128)(2,1)} %param.25) | copy-start | bytes 6291460
  28.9 4.6 %collective-permute-start.20 = (f32[96,256]{1,0:T(8,128)S(1)}, f32[96,256]{1,0:T(8,128)S(1)}, u32[]{:S(2)}, u32[]{:S(2)}) collective-permute-start(f32[96,256]{1,0:T(8,128)S(1)} %get-tuple-element.149.selected_ref), channel_id=1, source_target_pairs={{0,1},{1,0},{2,3},{3,2},{4,5},{5,4},{6,7},{7,6},{8,9},{9,8},{10,11... | collective-permute-start | bytes 294920 | tf_op jit(solution)/shard_map/ppermute | solution.py:33
  29.9 13.6 %copy-start.8 = (bf16[256,512]{1,0:T(8,128)(2,1)}, bf16[256,512]{1,0:T(8,128)(2,1)S(1)}, u32[]{:S(2)}) copy-start(bf16[256,512]{1,0:T(8,128)(2,1)S(1)} %get-tuple-element.262) | copy-start | bytes 786436
  29.9 13.6 %copy-start.9 = (bf16[256,512]{1,0:T(8,128)(2,1)}, bf16[256,512]{1,0:T(8,128)(2,1)S(1)}, u32[]{:S(2)}) copy-start(bf16[256,512]{1,0:T(8,128)(2,1)S(1)} %get-tuple-element.263) | copy-start | bytes 786436
  29.9 3.6 %copy-start.10 = (f32[16,1024]{1,0:T(8,128)S(1)}, f32[16,1024]{1,0:T(8,128)}, u32[]{:S(2)}) copy-start(f32[16,1024]{1,0:T(8,128)} %decay_log_ref.7) | copy-start | bytes 196612
  30.0 3.6 %copy-start.18 = (bf16[64,1024]{1,0:T(8,128)(2,1)S(1)}, bf16[64,1024]{1,0:T(8,128)(2,1)}, u32[]{:S(2)}) copy-start(bf16[64,1024]{1,0:T(8,128)(2,1)} %step_weight_ref.1) | copy-start | bytes 393220
  33.6 10.0 %copy-start.15 = (f32[96,256]{1,0:T(8,128)}, f32[96,256]{1,0:T(8,128)S(1)}, u32[]{:S(2)}) copy-start(f32[96,256]{1,0:T(8,128)S(1)} %collective-permute-done.20.other_ref) | copy-start | bytes 294916
  33.6 30.5 %copy-start.30 = (f32[1024]{0:T(1024)S(1)}, f32[1024]{0:T(1024)}, u32[]{:S(2)}) copy-start(f32[1024]{0:T(1024)} %param.24) | copy-start | bytes 12292
  43.6 1.7 collective-permute-start.22
  45.2 0.7 copy-start.26
  47.7 6.5 %collective-permute-start.23 = (f32[40,1024]{1,0:T(8,128)}, f32[40,1024]{1,0:T(8,128)S(1)}, u32[]{:S(2)}, u32[]{:S(2)}) collective-permute-start(f32[40,1024]{1,0:T(8,128)} %get-tuple-element.154.own_ref), channel_id=1, source_target_pairs={{0,4},{2,6},{4,0},{6,2},{8,12},{10,14},{12,8},{14,10},{16,20},{18,... | collective-permute-start | bytes 491528 | tf_op jit(solution)/shard_map/ppermute | solution.py:33
  54.1 0.7 copy-start.25
  56.6 6.8 %collective-permute-start.24 = (f32[16,1024]{1,0:T(8,128)}, f32[16,1024]{1,0:T(8,128)S(1)}, u32[]{:S(2)}, u32[]{:S(2)}) collective-permute-start(f32[16,1024]{1,0:T(8,128)} %get-tuple-element.157), channel_id=1, source_target_pairs={{0,8},{2,10},{4,12},{6,14},{8,16},{10,18},{12,20},{14,22},{16,24},... | collective-permute-start | bytes 196616 | tf_op jit(solution)/shard_map/ppermute | solution.py:28
  61.2 12.5 %collective-permute-start.25 = (f32[16,1024]{1,0:T(8,128)}, f32[16,1024]{1,0:T(8,128)S(1)}, u32[]{:S(2)}, u32[]{:S(2)}) collective-permute-start(f32[16,1024]{1,0:T(8,128)} %get-tuple-element.159), channel_id=1, source_target_pairs={{8,0},{10,2},{12,4},{14,6},{16,8},{18,10},{20,12},{22,14},{24,16},... | collective-permute-start | bytes 196616 | tf_op jit(solution)/shard_map/ppermute | solution.py:28
  73.7 0.6 copy-start.22
  74.3 3.2 %copy-start.3 = (bf16[256,1024]{1,0:T(8,128)(2,1)S(1)}, bf16[256,1024]{1,0:T(8,128)(2,1)}, u32[]{:S(2)}) copy-start(bf16[256,1024]{1,0:T(8,128)(2,1)} %get-tuple-element.161) | copy-start | bytes 1572868
  74.3 3.2 %copy-start.19 = (bf16[256,1024]{1,0:T(8,128)(2,1)S(1)}, bf16[256,1024]{1,0:T(8,128)(2,1)}, u32[]{:S(2)}) copy-start(bf16[256,1024]{1,0:T(8,128)(2,1)} %get-tuple-element.162) | copy-start | bytes 1572868
  103.1 5.6 %copy-start.14 = (f32[256,1024]{1,0:T(8,128)S(1)}, f32[256,1024]{1,0:T(8,128)}, u32[]{:S(2)}) copy-start(f32[256,1024]{1,0:T(8,128)} %get-tuple-element.75.convolved_ref) | copy-start | bytes 3145732 | tf_op jit(solution)/shard_map/cond
  103.1 5.6 %copy-start.17 = (bf16[96,1024]{1,0:T(8,128)(2,1)S(1)}, bf16[96,1024]{1,0:T(8,128)(2,1)}, u32[]{:S(2)}) copy-start(bf16[96,1024]{1,0:T(8,128)(2,1)} %get-tuple-element.73.select_ref) | copy-start | bytes 589828 | tf_op jit(solution)/shard_map/cond
  103.1 5.6 %collective-permute-start = (f32[96,256]{1,0:T(8,128)}, f32[96,256]{1,0:T(8,128)}, u32[]{:S(2)}, u32[]{:S(2)}) collective-permute-start(f32[96,256]{1,0:T(8,128)} %get-tuple-element.72.select_grad_ref.refs_1_), channel_id=1, source_target_pairs={{0,1},{1,0},{2,3},{3,2},{4,5},{5,4},{6,7},{7,6},{8,9},{9,8},{10,11... | collective-permute-start | bytes 294920 | tf_op jit(solution)/shard_map/cond/branch_1_fun/ppermute | solution.py:33
  106.6 9.6 %collective-permute-start.4 = (bf16[256,256]{1,0:T(8,128)(2,1)}, bf16[256,256]{1,0:T(8,128)(2,1)}, u32[]{:S(2)}, u32[]{:S(2)}) collective-permute-start(bf16[256,256]{1,0:T(8,128)(2,1)} %get-tuple-element.253), channel_id=1, source_target_pairs={{0,6},{2,4},{4,2},{6,0},{8,14},{10,12},{12,10},{14,8},{16,22},{18,... | collective-permute-start | bytes 393224 | tf_op jit(solution)/shard_map/cond/branch_1_fun/ppermute | solution.py:33
  106.6 9.6 %collective-permute-start.3 = (bf16[256,256]{1,0:T(8,128)(2,1)}, bf16[256,256]{1,0:T(8,128)(2,1)}, u32[]{:S(2)}, u32[]{:S(2)}) collective-permute-start(bf16[256,256]{1,0:T(8,128)(2,1)} %get-tuple-element.254), channel_id=1, source_target_pairs={{0,2},{2,0},{4,6},{6,4},{8,10},{10,8},{12,14},{14,12},{16,18},{18,... | collective-permute-start | bytes 393224 | tf_op jit(solution)/shard_map/cond/branch_1_fun/ppermute | solution.py:33
  107.3 8.9 %collective-permute-start.2 = (bf16[256,256]{1,0:T(8,128)(2,1)}, bf16[256,256]{1,0:T(8,128)(2,1)}, u32[]{:S(2)}, u32[]{:S(2)}) collective-permute-start(bf16[256,256]{1,0:T(8,128)(2,1)} %get-tuple-element.255), channel_id=1, source_target_pairs={{0,4},{2,6},{4,0},{6,2},{8,12},{10,14},{12,8},{14,10},{16,20},{18,... | collective-permute-start | bytes 393224 | tf_op jit(solution)/shard_map/cond/branch_1_fun/ppermute | solution.py:33
  112.7 11.7 %copy-start.20 = (bf16[256,1024]{1,0:T(8,128)(2,1)S(1)}, bf16[256,1024]{1,0:T(8,128)(2,1)}, u32[]{:S(2)}) copy-start(bf16[256,1024]{1,0:T(8,128)(2,1)} %get-tuple-element.81) | copy-start | bytes 1572868 | tf_op jit(solution)/shard_map/cond
  112.7 11.7 %copy-start.31 = (f32[1024]{0:T(1024)S(1)}, f32[1024]{0:T(1024)}, u32[]{:S(2)}) copy-start(f32[1024]{0:T(1024)} %get-tuple-element.85) | copy-start | bytes 12292 | tf_op jit(solution)/shard_map/cond
  112.7 3.4 %collective-permute-start.1 = (f32[8,1024]{1,0:T(8,128)}, f32[8,1024]{1,0:T(8,128)S(1)}, u32[]{:S(2)}, u32[]{:S(2)}) collective-permute-start(f32[8,1024]{1,0:T(8,128)} %get-tuple-element.79), channel_id=1, source_target_pairs={{2,0},{4,2},{6,4},{8,6},{10,8},{12,10},{14,12},{16,14},{18,16},{20... | collective-permute-start | bytes 98312 | tf_op jit(solution)/shard_map/cond/branch_1_fun/ppermute | solution.py:28
  118.2 21.7 %collective-permute-start.5 = (bf16[256,1024]{1,0:T(8,128)(2,1)}, bf16[256,1024]{1,0:T(8,128)(2,1)S(1)}, u32[]{:S(2)}, u32[]{:S(2)}) collective-permute-start(bf16[256,1024]{1,0:T(8,128)(2,1)} %patched.1.wait_ref.own_ref), channel_id=1, source_target_pairs={{0,4},{2,6},{4,0},{6,2},{8,12},{10,14},{12,8},{14,10},{16,20},{18,... | collective-permute-start | bytes 1572872 | tf_op jit(solution)/shard_map/cond/branch_1_fun/ppermute | solution.py:33
  122.3 8.6 %collective-permute-start.8 = (bf16[128,1024]{1,0:T(8,128)(2,1)}, bf16[128,1024]{1,0:T(8,128)(2,1)S(1)}, u32[]{:S(2)}, u32[]{:S(2)}) collective-permute-start(bf16[128,1024]{1,0:T(8,128)(2,1)} %get-tuple-element.89), channel_id=1, source_target_pairs={{0,2},{2,0},{4,6},{6,4},{8,10},{10,8},{12,14},{14,12},{16,18},{18,... | collective-permute-start | bytes 786440 | tf_op jit(solution)/shard_map/cond/branch_1_fun/ppermute | solution.py:33
  128.8 12.0 %copy-start.2 = (bf16[256,1024]{1,0:T(8,128)(2,1)S(1)}, bf16[256,1024]{1,0:T(8,128)(2,1)}, u32[]{:S(2)}) copy-start(bf16[256,1024]{1,0:T(8,128)(2,1)} %patched.1.wait_ref.own_ref) | copy-start | bytes 1572868 | tf_op jit(solution)/shard_map/cond
  128.8 5.0 %collective-permute-start.6 = (f32[1,1024]{1,0:T(1,128)S(1)}, f32[1,1024]{1,0:T(1,128)S(1)}, u32[]{:S(2)}, u32[]{:S(2)}) collective-permute-start(f32[1,1024]{1,0:T(1,128)S(1)} %bitcast.46), channel_id=1, source_target_pairs={{0,1},{1,0},{2,3},{3,2},{4,5},{5,4},{6,7},{7,6},{8,9},{9,8},{10,11... | collective-permute-start | bytes 12296 | tf_op jit(solution)/shard_map/cond/branch_1_fun/ppermute | solution.py:33
  129.7 4.6 %collective-permute-start.7 = (f32[1,256]{1,0:T(1,128)S(1)}, f32[1,256]{1,0:T(1,128)S(1)}, u32[]{:S(2)}, u32[]{:S(2)}) collective-permute-start(f32[1,256]{1,0:T(1,128)S(1)} %bitcast.49), channel_id=1, source_target_pairs={{0,1},{1,0},{2,3},{3,2},{4,5},{5,4},{6,7},{7,6},{8,9},{9,8},{10,11... | collective-permute-start | bytes 3080 | tf_op jit(solution)/shard_map/cond/branch_1_fun/ppermute | solution.py:33
  130.9 0.7 copy-start.24
  133.5 6.4 %collective-permute-start.9 = (bf16[64,1024]{1,0:T(8,128)(2,1)}, bf16[64,1024]{1,0:T(8,128)(2,1)S(1)}, u32[]{:S(2)}, u32[]{:S(2)}) collective-permute-start(bf16[64,1024]{1,0:T(8,128)(2,1)} %get-tuple-element.90), channel_id=1, source_target_pairs={{0,4},{2,6},{4,0},{6,2},{8,12},{10,14},{12,8},{14,10},{16,20},{18,... | collective-permute-start | bytes 393224 | tf_op jit(solution)/shard_map/cond/branch_1_fun/ppermute | solution.py:33
  134.4 5.6 %copy-start.34 = (f32[1,256]{1,0:T(1,128)}, f32[1,256]{1,0:T(1,128)S(1)}, u32[]{:S(2)}) copy-start(f32[1,256]{1,0:T(1,128)S(1)} %collective-permute-done.7.refs_2_) | copy-start | bytes 3076 | tf_op jit(solution)/shard_map/cond
  139.9 0.7 copy-start.21
  139.9 0.9 copy-start.4
  140.8 3.4 %copy-start.35 = (f32[1,256]{1,0:T(1,128)S(1)}, f32[1,256]{1,0:T(1,128)}, u32[]{:S(2)}) copy-start(f32[1,256]{1,0:T(1,128)} %copy-done.34) | copy-start | bytes 3076 | tf_op jit(solution)/shard_map/cond
  143.0 2.9 %collective-permute-start.10 = (bf16[512,1024]{1,0:T(8,128)(2,1)}, bf16[512,1024]{1,0:T(8,128)(2,1)S(1)}, u32[]{:S(2)}, u32[]{:S(2)}) collective-permute-start(bf16[512,1024]{1,0:T(8,128)(2,1)} %pad_maximum_fusion), channel_id=1, source_target_pairs={{0,2},{2,0},{4,6},{6,4},{8,10},{10,8},{12,14},{14,12},{16,18},{18,... | collective-permute-start | bytes 3145736 | tf_op jit(solution)/shard_map/cond/branch_1_fun/ppermute | solution.py:33
  145.9 1.1 copy-start.12
  146.9 8.7 %copy-start.1 = (bf16[1024,1024]{1,0:T(8,128)(2,1)S(1)}, bf16[1024,1024]{1,0:T(8,128)(2,1)}, u32[]{:S(2)}) copy-start(bf16[1024,1024]{1,0:T(8,128)(2,1)} %get-tuple-element.98) | copy-start | bytes 6291460 | tf_op jit(solution)/shard_map/cond
  150.6 13.5 %collective-permute-start.11 = (bf16[80,1024]{1,0:T(8,128)(2,1)}, bf16[80,1024]{1,0:T(8,128)(2,1)S(1)}, u32[]{:S(2)}, u32[]{:S(2)}) collective-permute-start(bf16[80,1024]{1,0:T(8,128)(2,1)} %get-tuple-element.93), channel_id=1, source_target_pairs={{0,8},{2,10},{4,12},{6,14},{8,0},{10,2},{12,4},{14,6},{16,24},{18,... | collective-permute-start | bytes 491528 | tf_op jit(solution)/shard_map/cond/branch_1_fun/ppermute | solution.py:33
  153.0 16.5 %collective-permute-start.12 = (bf16[80,1024]{1,0:T(8,128)(2,1)}, bf16[80,1024]{1,0:T(8,128)(2,1)S(1)}, u32[]{:S(2)}, u32[]{:S(2)}) collective-permute-start(bf16[80,1024]{1,0:T(8,128)(2,1)} %get-tuple-element.94), channel_id=1, source_target_pairs={{0,16},{2,18},{4,20},{6,22},{8,24},{10,26},{12,28},{14,30},{16,0},... | collective-permute-start | bytes 491528 | tf_op jit(solution)/shard_map/cond/branch_1_fun/ppermute | solution.py:33
  155.6 13.9 %collective-permute-start.13 = (bf16[80,1024]{1,0:T(8,128)(2,1)}, bf16[80,1024]{1,0:T(8,128)(2,1)S(1)}, u32[]{:S(2)}, u32[]{:S(2)}) collective-permute-start(bf16[80,1024]{1,0:T(8,128)(2,1)} %get-tuple-element.95), channel_id=1, source_target_pairs={{0,24},{2,26},{4,28},{6,30},{8,16},{10,18},{12,20},{14,22},{16,8},... | collective-permute-start | bytes 491528 | tf_op jit(solution)/shard_map/cond/branch_1_fun/ppermute | solution.py:33
  155.6 13.9 %copy-start.11 = (f32[80,1024]{1,0:T(8,128)S(1)}, f32[80,1024]{1,0:T(8,128)}, u32[]{:S(2)}) copy-start(f32[80,1024]{1,0:T(8,128)} %get-tuple-element.92.refs_1_) | copy-start | bytes 983044 | tf_op jit(solution)/shard_map/cond
  169.6 15.6 %collective-permute-start.16 = (bf16[80,1024]{1,0:T(8,128)(2,1)S(1)}, bf16[80,1024]{1,0:T(8,128)(2,1)S(1)}, u32[]{:S(2)}, u32[]{:S(2)}) collective-permute-start(bf16[80,1024]{1,0:T(8,128)(2,1)S(1)} %pad_maximum_fusion.4), channel_id=1, source_target_pairs={{0,8},{2,10},{4,12},{6,14},{8,0},{10,2},{12,4},{14,6},{16,24},{18,... | collective-permute-start | bytes 491528 | tf_op jit(solution)/shard_map/cond/branch_1_fun/ppermute | solution.py:33
  175.9 14.9 %collective-permute-start.15 = (bf16[80,1024]{1,0:T(8,128)(2,1)S(1)}, bf16[80,1024]{1,0:T(8,128)(2,1)S(1)}, u32[]{:S(2)}, u32[]{:S(2)}) collective-permute-start(bf16[80,1024]{1,0:T(8,128)(2,1)S(1)} %pad_maximum_fusion.4), channel_id=1, source_target_pairs={{0,16},{2,18},{4,20},{6,22},{8,24},{10,26},{12,28},{14,30},{16,0},... | collective-permute-start | bytes 491528 | tf_op jit(solution)/shard_map/cond/branch_1_fun/ppermute | solution.py:33
  177.0 22.0 %collective-permute-start.14 = (bf16[80,1024]{1,0:T(8,128)(2,1)S(1)}, bf16[80,1024]{1,0:T(8,128)(2,1)S(1)}, u32[]{:S(2)}, u32[]{:S(2)}) collective-permute-start(bf16[80,1024]{1,0:T(8,128)(2,1)S(1)} %pad_maximum_fusion.4), channel_id=1, source_target_pairs={{0,24},{2,26},{4,28},{6,30},{8,16},{10,18},{12,20},{14,22},{16,8},... | collective-permute-start | bytes 491528 | tf_op jit(solution)/shard_map/cond/branch_1_fun/ppermute | solution.py:33
  200.1 14.3 %collective-permute-start.28 = (bf16[320,1024]{1,0:T(8,128)(2,1)}, bf16[320,1024]{1,0:T(8,128)(2,1)S(1)}, u32[]{:S(2)}, u32[]{:S(2)}) collective-permute-start(bf16[320,1024]{1,0:T(8,128)(2,1)} %get-tuple-element.171.first_ref.rest_0_), channel_id=1, source_target_pairs={{0,4},{2,6},{4,0},{6,2},{8,12},{10,14},{12,8},{14,10},{16,20},{18,... | collective-permute-start | bytes 1966088 | tf_op jit(solution)/shard_map/ppermute | solution.py:33
  201.4 28.0 %collective-permute-start.30 = (bf16[320,1024]{1,0:T(8,128)(2,1)}, bf16[320,1024]{1,0:T(8,128)(2,1)S(1)}, u32[]{:S(2)}, u32[]{:S(2)}) collective-permute-start(bf16[320,1024]{1,0:T(8,128)(2,1)} %get-tuple-element.171.first_ref.rest_0_), channel_id=1, source_target_pairs={{0,2},{2,0},{4,6},{6,4},{8,10},{10,8},{12,14},{14,12},{16,18},{18,... | collective-permute-start | bytes 1966088 | tf_op jit(solution)/shard_map/ppermute | solution.py:33
  201.4 15.6 %collective-permute-start.26 = (f32[256,512]{1,0:T(8,128)}, f32[256,512]{1,0:T(8,128)S(1)}, u32[]{:S(2)}, u32[]{:S(2)}) collective-permute-start(f32[256,512]{1,0:T(8,128)} %get-tuple-element.167), channel_id=1, source_target_pairs={{0,1},{1,0},{2,3},{3,2},{4,5},{5,4},{6,7},{7,6},{8,9},{9,8},{10,11... | collective-permute-start | bytes 1572872 | tf_op jit(solution)/shard_map/ppermute | solution.py:33
  202.0 25.2 %collective-permute-start.27 = (f32[256,512]{1,0:T(8,128)}, f32[256,512]{1,0:T(8,128)S(1)}, u32[]{:S(2)}, u32[]{:S(2)}) collective-permute-start(f32[256,512]{1,0:T(8,128)} %get-tuple-element.169), channel_id=1, source_target_pairs={{0,1},{1,0},{2,3},{3,2},{4,5},{5,4},{6,7},{7,6},{8,9},{9,8},{10,11... | collective-permute-start | bytes 1572872 | tf_op jit(solution)/shard_map/ppermute | solution.py:33
  214.4 21.4 %copy-start.5 = (bf16[320,1024]{1,0:T(8,128)(2,1)}, bf16[320,1024]{1,0:T(8,128)(2,1)S(1)}, u32[]{:S(2)}) copy-start(bf16[320,1024]{1,0:T(8,128)(2,1)S(1)} %collective-permute-done.28.first_ref.rest_2_) | copy-start | bytes 1966084
  214.4 21.4 %collective-permute-start.29 = (bf16[320,1024]{1,0:T(8,128)(2,1)S(1)}, bf16[320,1024]{1,0:T(8,128)(2,1)S(1)}, u32[]{:S(2)}, u32[]{:S(2)}) collective-permute-start(bf16[320,1024]{1,0:T(8,128)(2,1)S(1)} %collective-permute-done.28.first_ref.rest_2_), channel_id=1, source_target_pairs={{0,2},{2,0},{4,6},{6,4},{8,10},{10,8},{12,14},{14,12},{16,18},{18,... | collective-permute-start | bytes 1966088 | tf_op jit(solution)/shard_map/ppermute | solution.py:33
  229.3 0.9 copy-start.7
  235.8 0.8 copy-start.6
  (4 other events, 2.5 us)
Sparse Core Ops, SparseCore 0:
  79.8 133.3 all-reduce.2

commit v18 on v16

--- a/solution.py
+++ b/solution.py
@@ -209,6 +209,24 @@
     return pltpu.roll(tile, lax.rem(lanes - back, lanes), 1)
 
 
+def put_ends(ends_ref, state, adjoint, total):
+    count, width = state.shape
+    ends_ref[:count, :] = state.astype(bf16)
+    ends_ref[count : 2 * count, :] = adjoint.astype(bf16)
+    high = total.astype(bf16).astype(f32)
+    upper = lax.broadcasted_iota(jnp.int32, (16, width), 0) < 8
+    ends_ref[2 * count :, :] = jnp.where(upper, high, total - high).astype(bf16)
+
+
+def get_ends(ends_ref, count):
+    total = ends_ref[2 * count :].astype(f32)
+    return (
+        ends_ref[:count].astype(f32),
+        ends_ref[count : 2 * count].astype(f32),
+        total[:1] + total[8:9],
+    )
+
+
 def ends_kernel(
     selected_ref,
     other_ref,
@@ -258,10 +276,7 @@
         return state, product, adjoint
 
     state, product, adjoint = lax.fori_loop(0, rows // body_rows, body, (zero, zero + 1.0, zero))
-    ends_ref[:count, :] = state
-    ends_ref[count : 2 * count, :] = adjoint
-    total = jnp.sum(held_step[...], axis=0, keepdims=True)
-    ends_ref[2 * count :, :] = jnp.broadcast_to(total, (8, total.shape[1]))
+    put_ends(ends_ref, state, adjoint, jnp.sum(held_step[...], axis=0, keepdims=True))
 
 
 def scan_ends(
@@ -286,11 +301,11 @@
             whole_spec(rows, masks.shape[1]),
             column_spec(count),
         ],
-        [column_spec(rows), column_spec(rows), column_spec(2 * count + 8)],
+        [column_spec(rows), column_spec(rows), column_spec(2 * count + 16)],
         [
             jax.ShapeDtypeStruct((rows, width), f32),
             jax.ShapeDtypeStruct((rows, width), f32),
-            jax.ShapeDtypeStruct((2 * count + 8, width), f32),
+            jax.ShapeDtypeStruct((2 * count + 16, width), bf16),
         ],
         [pltpu.VMEM((2 * count, rows), f32)] + [pltpu.VMEM((rows, scan_width), f32)] * 3,
         selected,
@@ -371,7 +386,7 @@
     decay = -jnp.exp(decay_log_ref[...])
     decay2 = decay * log2e
     before_steps = passed_ref[2 * count : 2 * count + 1, :]
-    entry = passed_ref[:count, :] + through(decay, before_steps) * entering_ref[...]
+    entry = passed_ref[:count, :] + through(decay, before_steps) * entering_ref[...].astype(f32)
     entry_ref[...] = entry
     coef[...] = selected_ref[rank:, :] + other_ref[rank:, :]
     act = act_ref[...].astype(f32)
@@ -481,7 +496,7 @@
     decay = -jnp.exp(decay_log_ref[...])
     decay2 = decay * log2e
     after_steps = passed_ref[2 * count + 1 : 2 * count + 2, :]
-    tail = passed_ref[count : 2 * count, :] + through(decay, after_steps) * returning_ref[...]
+    tail = passed_ref[count : 2 * count, :] + through(decay, after_steps) * returning_ref[...].astype(f32)
     selected = selected_ref[...] + other_ref[...]
     coef[...] = selected[rank:, :]
     step_low = selected[:rank, :].astype(bf16)
@@ -1078,22 +1093,16 @@
     new_passed_ref, *ends_refs = rest if first else rest[1:]
     decay = -jnp.exp(decay_log_ref[...])
     second = second_ref[0] > 0
-
-    def split(ref):
-        return ref[:count], ref[count : 2 * count], ref[2 * count : 2 * count + 1]
-
-    own, other = split(own_ref), split(other_ref)
+    own, other = get_ends(own_ref, count), get_ends(other_ref, count)
     early = [jnp.where(second, b, a) for a, b in zip(own, other)]
     late = [jnp.where(second, a, b) for a, b in zip(own, other)]
     state = late[0] + through(decay, late[2]) * early[0]
     adjoint = early[1] + through(decay, early[2]) * late[1]
     if len(ends_refs) == 2:
-        ends_refs[0][...] = state
-        ends_refs[1][...] = adjoint
+        ends_refs[0][...] = state.astype(bf16)
+        ends_refs[1][...] = adjoint.astype(bf16)
     else:
-        ends_refs[0][:count, :] = state
-        ends_refs[0][count : 2 * count, :] = adjoint
-        ends_refs[0][2 * count :, :] = jnp.broadcast_to(early[2] + late[2], (8, decay.shape[1]))
+        put_ends(ends_refs[0], state, adjoint, early[2] + late[2])
     if first:
         before = after = jnp.zeros((count, width), f32)
         before_steps = after_steps = jnp.zeros((1, width), f32)
@@ -1112,11 +1121,11 @@
 def carried(ends, decay_log):
     count, width = decay_log.shape
     place = lax.axis_index("wide").astype(jnp.int32)
-    state = jax.ShapeDtypeStruct((count, width), f32)
+    state = jax.ShapeDtypeStruct((count, width), bf16)
     passed_kind = jax.ShapeDtypeStruct((2 * count + 8, width), f32)
     packed, passed = ends, []
     vmem = pl.BlockSpec(memory_space=pltpu.VMEM)
-    for k, kinds in enumerate(([jax.ShapeDtypeStruct(ends.shape, f32)], [state, state])):
+    for k, kinds in enumerate(([jax.ShapeDtypeStruct(ends.shape, bf16)], [state, state])):
         new_passed, *out = pl.pallas_call(
             functools.partial(round_kernel, first=k == 0),
             in_specs=[pl.BlockSpec(memory_space=pltpu.SMEM)] + [vmem] * (3 + k),
@@ -1306,7 +1315,7 @@
 
     core = swapped(held, "wide", 1)
     begun, out_weight_grad = joined_first(four_place, gate_sum, held, core, out_sum)
-    near = after(swapped(held, "wide", 2), begun)
+    near = swapped(held, "wide", 2)
     far = swapped(near, "wide", 1)
     conv_at = rank + count + 2
     (

time: 236 us -> 234 us (level)
    psum x1, waiting for transfers between devices: 9.35 us -> 0.02 us  [local(): out_sum, gate_sum = lax.psum(products, 'wide')]
    ppermute x26, waiting for transfers between devices: 52.4 us -> 60.1 us  [swapped(): return lax.ppermute(array, axis, [(i, i ^ bit) for i in range(peers)])]
    unnamed x44 -> x40, local copies, waits for them, and re-layouts: 5.04 us -> 4.35 us
  transfers between devices with their start and end apart: 32 -> 32, of which waited for: 15 -> 13; matrix products, arithmetic and copies ran while one was open for 8% -> 8% of each run, Pallas kernels for 25% -> 25%
where the time goes in v18:
time: 234 us; the launch traced here: 233 us
  Pallas kernels  77.5 us (33%)
  waiting for transfers between devices  61.3 us (26%)
  starting transfers between devices  47 us (20%)
  matrix products  15 us (6%)
  between operations  14.3 us (6%)
  local copies, waits for them, and re-layouts  11.3 us (5%)
  other arithmetic  6 us (3%)
    ppermute x26, waiting for transfers between devices, swapped(): return lax.ppermute(array, axis, [(i, i ^ bit) for i in range(peers)])  60.1 us
    pallas_call x5, Pallas kernels, call(): pl.pallas_call(kernel, grid=(width // scan_width,), in_specs=in_specs, ou...  50.3 us
    ppermute x26, starting transfers between devices, swapped(): return lax.ppermute(array, axis, [(i, i ^ bit) for i in range(peers)])  33.9 us
    ppermute x4, starting transfers between devices, passed_along(): return lax.ppermute(array, axis, pairs)  11.7 us
    pallas_call x2, Pallas kernels, joined(): pl.pallas_call(kernel, grid_spec=pltpu.PrefetchScalarGridSpec(num_scalar_...  10.9 us
  transfers between devices with their start and end apart: 32, of which 13 were waited for; matrix products, arithmetic and copies ran while one was open for 8% of the time, Pallas kernels for 25%

profile of v18, /device:TPU:0, one launch (start us, length us, event | category | flops | bytes accessed | tf_op | source)
XLA Modules:
  0.0 232.7 jit_solution(14388205061990467328)
XLA Ops:
  7.2 3.0 %collective-permute-start.19 = (bf16[256,512]{1,0:T(8,128)(2,1)}, bf16[256,512]{1,0:T(8,128)(2,1)S(1)}, u32[]{:S(2)}, u32[]{:S(2)}) collective-permute-start(bf16[256,512]{1,0:T(8,128)(2,1)} %own_ref.1), channel_id=1, source_target_pairs={{0,1},{1,0},{2,3},{3,2},{4,5},{5,4},{6,7},{7,6},{8,9},{9,8},{10,11... | collective-permute-start | bytes 786440 | tf_op jit(solution)/shard_map/ppermute | solution.py:33
  10.3 1.4 edge_rows.1
  11.6 1.3 collective-permute-start.21
  13.0 4.0 %collective-permute-start.20 = (bf16[16,512]{1,0:T(8,128)(2,1)}, bf16[16,512]{1,0:T(8,128)(2,1)S(1)}, u32[]{:S(2)}, u32[]{:S(2)}) collective-permute-start(bf16[16,512]{1,0:T(8,128)(2,1)} %edge_rows.1), channel_id=1, source_target_pairs={{0,2},{2,4},{4,6},{6,8},{8,10},{10,12},{12,14},{14,16},{16,18},{18... | collective-permute-start | bytes 49160 | tf_op jit(solution)/shard_map/ppermute | solution.py:28
  17.0 1.6 collective-permute-start.23
  19.3 2.5 %normalized.1 = (bf16[256,1024]{1,0:T(8,128)(2,1)}, bf16[272,1024]{1,0:T(8,128)(2,1)}, bf16[256,1024]{1,0:T(8,128)(2,1)}, f32[256,1]{1,0:T(8,128)}, f32[256,128]{1,0:T(8,128)S(1)}) custom-call(bf16[256,512]{1,0:T(8,128)(2,1)} %own_ref.1, bf16[256,512]{1,0:T(8,128)(2,1)} %copy-done.27, bf16[16,512]{1,0:T(8,128)(2,1)} %copy-done.36, ...), custom_call_target="tpu_custom_call" | custom-call | flops 1 | bytes 1 | tf_op jit(solution)/shard_map/normalized/pallas_call | solution.py:783
  21.8 4.0 %fusion.25.inner_ref.gate_ref = bf16[2,272,1024]{2,1,0:T(8,128)(2,1)S(1)} fusion(bf16[1024,2,1024]{2,1,0:T(2,128)(2,1)} %param.17, bf16[272,1024]{1,0:T(8,128)(2,1)} %get-tuple-element.150), kind=kOutput, calls=%fused_computation.49 | convolution fusion | flops 1141407744 | bytes 5865472 | tf_op jit(solution)/shard_map/td,dce->cte/dot_general | solution.py:1176
  25.8 3.1 %convolve.1 = (f32[256,1024]{1,0:T(8,128)}, bf16[256,1024]{1,0:T(8,128)(2,1)S(1)}, f32[96,256]{1,0:T(8,128)S(1)}) custom-call(bf16[2,272,1024]{2,1,0:T(8,128)(2,1)S(1)} %fusion.25.inner_ref.gate_ref, f32[4,1024]{1,0:T(4,128)S(1)} %copy-done.31, f32[1,1024]{1,0:T(1,128)} %bitcast.44, bf16[96,1024]{1,0:T(8,128)(2,1)S(1)} %copy-done.21, ...), custom_call_target="tpu_custom_call" | custom-call | flops 1 | bytes 1 | tf_op jit(solution)/shard_map/convolve/pallas_call | solution.py:127
  28.9 0.9 collective-permute-start.22
  30.7 2.8 %collective-permute-done.22.other_ref = f32[96,256]{1,0:T(8,128)S(1)} collective-permute-done((f32[96,256]{1,0:T(8,128)S(1)}, f32[96,256]{1,0:T(8,128)S(1)}, u32[]{:S(2)}, u32[]{:S(2)}) %collective-permute-start.22) | collective-permute-done | bytes 98336 | tf_op jit(solution)/shard_map/ppermute | solution.py:33
  33.5 10.0 %scan_ends.1 = (f32[256,1024]{1,0:T(8,128)}, f32[256,1024]{1,0:T(8,128)}, bf16[48,1024]{1,0:T(8,128)(2,1)}) custom-call(f32[96,256]{1,0:T(8,128)S(1)} %get-tuple-element.152.selected_ref, f32[96,256]{1,0:T(8,128)S(1)} %collective-permute-done.22.other_ref, bf16[64,1024]{1,0:T(8,128)(2,1)S(1)} %copy-done.23, f32[1,1024]{1,0:T(1,128)} %bitcast.45, ...), custom_call_target="tpu_custom_call" | custom-call | flops 1 | bytes 1 | tf_op jit(solution)/shard_map/scan_ends/pallas_call | solution.py:127
  43.6 1.5 collective-permute-done.24.other_ref
  45.7 1.7 carry_round.2
  47.4 1.7 collective-permute-start.25
  49.1 3.4 %collective-permute-done.25.other_ref = bf16[48,1024]{1,0:T(8,128)(2,1)S(1)} collective-permute-done((bf16[48,1024]{1,0:T(8,128)(2,1)}, bf16[48,1024]{1,0:T(8,128)(2,1)S(1)}, u32[]{:S(2)}, u32[]{:S(2)}) %collective-permute-start.25) | collective-permute-done | bytes 98336 | tf_op jit(solution)/shard_map/ppermute | solution.py:33
  53.1 1.8 carry_round.3
  54.9 4.6 %collective-permute-start.26 = (bf16[16,1024]{1,0:T(8,128)(2,1)}, bf16[16,1024]{1,0:T(8,128)(2,1)S(1)}, u32[]{:S(2)}, u32[]{:S(2)}) collective-permute-start(bf16[16,1024]{1,0:T(8,128)(2,1)} %get-tuple-element.160), channel_id=1, source_target_pairs={{0,8},{2,10},{4,12},{6,14},{8,16},{10,18},{12,20},{14,22},{16,24},... | collective-permute-start | bytes 98312 | tf_op jit(solution)/shard_map/ppermute | solution.py:28
  59.5 1.5 collective-permute-start.27
  62.0 9.7 %scan_forward.1 = (bf16[256,1024]{1,0:T(8,128)(2,1)S(1)}, bf16[256,1024]{1,0:T(8,128)(2,1)}, f32[16,1024]{1,0:T(8,128)}) custom-call(f32[96,256]{1,0:T(8,128)S(1)} %get-tuple-element.152.selected_ref, f32[96,256]{1,0:T(8,128)} %copy-done.20, f32[256,1024]{1,0:T(8,128)} %get-tuple-element.155.step_ref, bf16[256,1024]{1,0:T(8,128)(2,1)S(1)} %get-tuple-element.153.act_ref, ...), custom_call_target="tpu_custom_call" | custom-call | flops 1 | bytes 1 | tf_op jit(solution)/shard_map/scan_forward/pallas_call | solution.py:127
  71.7 3.2 %convolution_convert_fusion = bf16[1024,1024]{1,0:T(8,128)(2,1)} fusion(bf16[256,1024]{1,0:T(8,128)(2,1)S(1)} %after.9, bf16[256,512]{1,0:T(8,128)(2,1)} %copy-done.12, bf16[256,512]{1,0:T(8,128)(2,1)} %copy-done.11), kind=kOutput, calls=%fused_computation.46 | convolution fusion | flops 538968064 | bytes 3145728 | tf_op jit(solution)/shard_map/dot_general | solution.py:1214
  74.9 2.1 convolution_convert_fusion.1
  77.0 122.0 %conditional.1 = (bf16[320,1024]{1,0:T(8,128)(2,1)}, bf16[256,512]{1,0:T(8,128)(2,1)}, bf16[256,512]{1,0:T(8,128)(2,1)}) conditional(s32[]{:T(128)} %convert_element_type.49, () %tuple.16, (s32[]{:T(128)}, f32[1024]{0:T(1024)}, f32[96,256]{1,0:T(8,128)S(1)}, f32[96,256]{1,0:T(8,128)}, f32[256,1024]{1,0:T(8,128)}, /*index=5*/f32[256,1024]{1,0:T(8,128)}, ...), branch_computations={%region_0.1_spmd, %region_1.4_spmd} | conditional | flops 1621776640 | bytes 85772024 | solution.py:1309
  77.0 23.5 %scan_backward.1 = (f32[256,1024]{1,0:T(8,128)}, f32[96,256]{1,0:T(8,128)}, f32[82,1024]{1,0:T(8,128)}) custom-call(f32[96,256]{1,0:T(8,128)S(1)} %get-tuple-element.62.selected_ref, f32[96,256]{1,0:T(8,128)} %get-tuple-element.63.other_ref, f32[256,1024]{1,0:T(8,128)} %get-tuple-element.64.step_pre_ref, f32[256,1024]{1,0:T(8,128)} %get-tuple-element.65.step_ref, ...), custom_call_target="tpu_custom_call" | custom-call | flops 1 | bytes 1 | tf_op jit(solution)/shard_map/cond/branch_1_fun/scan_backward/pallas_call | solution.py:127
  100.6 1.5 collective-permute-start
  102.1 1.9 constant_dynamic-slice_fusion
  104.7 1.4 collective-permute-start.2
  106.1 4.0 %convolve_grad.1 = (bf16[256,1024]{1,0:T(8,128)(2,1)}, f32[8,1024]{1,0:T(8,128)}, f32[8,1024]{1,0:T(8,128)}, f32[101,1024]{1,0:T(8,128)}) custom-call(f32[96,256]{1,0:T(8,128)} %get-tuple-element.76.select_grad_ref.refs_1_, f32[96,256]{1,0:T(8,128)} %collective-permute-done.other_ref, bf16[96,1024]{1,0:T(8,128)(2,1)S(1)} %copy-done.22, ...), custom_call_target="tpu_custom_call" | custom-call | flops 1 | bytes 1 | tf_op jit(solution)/shard_map/cond/branch_1_fun/convolve_grad/pallas_call | solution.py:127
  110.2 1.6 collective-permute-start.1
  111.8 1.0 copy.34
  114.2 1.4 patched.1.wait_ref.own_ref
  115.7 1.8 collective-permute-start.5
  117.5 2.2 small_halves.1
  119.7 2.1 collective-permute-start.8
  121.8 4.4 %fusion.7 = (f32[256]{0:T(256)S(1)}, f32[1024]{0:T(1024)S(1)}, f32[256,1024]{1,0:T(8,128)S(1)}) fusion(bf16[256,1024]{1,0:T(8,128)(2,1)} %get-tuple-element.87, f32[1024]{0:T(1024)S(1)} %copy-done.34, f32[256]{0:T(256)S(1)} %bitcast.42, bf16[1024,2,1024]{2,1,0:T(2,128)(2,1)} %get-tuple-element.204, bf16[1,256,1024]{2,1,0:T(8,128)(2,1)S(1)} %bitcast.37, ...), kind=kOutput, calls=%fused_computation.7 | convolution fusion | flops 1076099840 | bytes 6825984 | tf_op jit(solution)/shard_map/cond/branch_1_fun/cte,dce->td/dot_general | solution.py:1262
  126.2 1.0 collective-permute-start.6
  127.2 1.1 collective-permute-start.7
  129.0 1.9 folded.1
  131.8 5.6 %collective-permute-done.9.refs_3_.arrived_ref = bf16[64,1024]{1,0:T(8,128)(2,1)S(1)} collective-permute-done((bf16[64,1024]{1,0:T(8,128)(2,1)}, bf16[64,1024]{1,0:T(8,128)(2,1)S(1)}, u32[]{:S(2)}, u32[]{:S(2)}) %collective-permute-start.9) | collective-permute-done | bytes 131104 | tf_op jit(solution)/shard_map/cond/branch_1_fun/ppermute | solution.py:33
  138.2 2.1 pad_maximum_fusion
  140.3 0.9 slice_select_fusion.refs_0_
  141.2 1.9 collective-permute-done.10.far_ref
  143.2 1.0 copy-done.16
  144.2 3.5 %inner_quarter.1 = (f32[80,1024]{1,0:T(8,128)}, bf16[80,1024]{1,0:T(8,128)(2,1)}, bf16[80,1024]{1,0:T(8,128)(2,1)}, bf16[80,1024]{1,0:T(8,128)(2,1)}) custom-call(s32[1]{0:T(128)} %bitcast.place_ref, bf16[256,1024]{1,0:T(8,128)(2,1)} %patched.1.wait_ref.own_ref, bf16[256,1024]{1,0:T(8,128)(2,1)} %after.6.near_ref, bf16[512,1024]{1,0:T(8,128)(2,1)} %copy-done.16, ...), custom_call_target="tpu_custom_call" | custom-call | flops 1 | bytes 1 | tf_op jit(solution)/shard_map/cond/branch_1_fun/inner_quarter/pallas_call | solution.py:964
  147.7 0.9 copy-done.41
  148.5 2.4 %collective-permute-start.11 = (bf16[80,1024]{1,0:T(8,128)(2,1)S(1)}, bf16[80,1024]{1,0:T(8,128)(2,1)S(1)}, u32[]{:S(2)}, u32[]{:S(2)}) collective-permute-start(bf16[80,1024]{1,0:T(8,128)(2,1)S(1)} %copy-done.41), channel_id=1, source_target_pairs={{0,8},{2,10},{4,12},{6,14},{8,0},{10,2},{12,4},{14,6},{16,24},{18,... | collective-permute-start | bytes 491528 | tf_op jit(solution)/shard_map/cond/branch_1_fun/ppermute | solution.py:33
  151.0 2.6 %collective-permute-start.12 = (bf16[80,1024]{1,0:T(8,128)(2,1)S(1)}, bf16[80,1024]{1,0:T(8,128)(2,1)S(1)}, u32[]{:S(2)}, u32[]{:S(2)}) collective-permute-start(bf16[80,1024]{1,0:T(8,128)(2,1)S(1)} %copy-done.40), channel_id=1, source_target_pairs={{0,16},{2,18},{4,20},{6,22},{8,24},{10,26},{12,28},{14,30},{16,0},... | collective-permute-start | bytes 491528 | tf_op jit(solution)/shard_map/cond/branch_1_fun/ppermute | solution.py:33
  154.3 7.1 %collective-permute-done.11 = bf16[80,1024]{1,0:T(8,128)(2,1)S(1)} collective-permute-done((bf16[80,1024]{1,0:T(8,128)(2,1)S(1)}, bf16[80,1024]{1,0:T(8,128)(2,1)S(1)}, u32[]{:S(2)}, u32[]{:S(2)}) %collective-permute-start.11) | collective-permute-done | bytes 163872 | tf_op jit(solution)/shard_map/cond/branch_1_fun/ppermute | solution.py:33
  161.4 5.3 %collective-permute-done.13 = bf16[80,1024]{1,0:T(8,128)(2,1)S(1)} collective-permute-done((bf16[80,1024]{1,0:T(8,128)(2,1)S(1)}, bf16[80,1024]{1,0:T(8,128)(2,1)S(1)}, u32[]{:S(2)}, u32[]{:S(2)}) %collective-permute-start.13) | collective-permute-done | bytes 163872 | tf_op jit(solution)/shard_map/cond/branch_1_fun/ppermute | solution.py:33
  166.9 5.5 %collective-permute-start.16 = (bf16[80,1024]{1,0:T(8,128)(2,1)S(1)}, bf16[80,1024]{1,0:T(8,128)(2,1)S(1)}, u32[]{:S(2)}, u32[]{:S(2)}) collective-permute-start(bf16[80,1024]{1,0:T(8,128)(2,1)S(1)} %pad_maximum_fusion.4), channel_id=1, source_target_pairs={{0,8},{2,10},{4,12},{6,14},{8,0},{10,2},{12,4},{14,6},{16,24},{18,... | collective-permute-start | bytes 491528 | tf_op jit(solution)/shard_map/cond/branch_1_fun/ppermute | solution.py:33
  172.5 1.2 collective-permute-start.17
  173.7 0.9 collective-permute-start.18
  174.5 1.4 collective-permute-start.15
  175.9 1.4 collective-permute-start.14
  177.4 5.2 %collective-permute-done.16 = bf16[80,1024]{1,0:T(8,128)(2,1)S(1)} collective-permute-done((bf16[80,1024]{1,0:T(8,128)(2,1)S(1)}, bf16[80,1024]{1,0:T(8,128)(2,1)S(1)}, u32[]{:S(2)}, u32[]{:S(2)}) %collective-permute-start.16) | collective-permute-done | bytes 163872 | tf_op jit(solution)/shard_map/cond/branch_1_fun/ppermute | solution.py:33
  182.7 7.4 %collective-permute-done.15 = bf16[80,1024]{1,0:T(8,128)(2,1)S(1)} collective-permute-done((bf16[80,1024]{1,0:T(8,128)(2,1)S(1)}, bf16[80,1024]{1,0:T(8,128)(2,1)S(1)}, u32[]{:S(2)}, u32[]{:S(2)}) %collective-permute-start.15) | collective-permute-done | bytes 163872 | tf_op jit(solution)/shard_map/cond/branch_1_fun/ppermute | solution.py:33
  190.1 6.7 %collective-permute-done.14 = bf16[80,1024]{1,0:T(8,128)(2,1)S(1)} collective-permute-done((bf16[80,1024]{1,0:T(8,128)(2,1)S(1)}, bf16[80,1024]{1,0:T(8,128)(2,1)S(1)}, u32[]{:S(2)}, u32[]{:S(2)}) %collective-permute-start.14) | collective-permute-done | bytes 163872 | tf_op jit(solution)/shard_map/cond/branch_1_fun/ppermute | solution.py:33
  197.0 0.9 pad_maximum_fusion.1
  197.9 1.0 fusion.15
  199.0 1.1 collective-permute-start.28
  200.1 13.1 %collective-permute-done.28.first_ref.rest_2_ = bf16[320,1024]{1,0:T(8,128)(2,1)S(1)} collective-permute-done((bf16[320,1024]{1,0:T(8,128)(2,1)}, bf16[320,1024]{1,0:T(8,128)(2,1)S(1)}, u32[]{:S(2)}, u32[]{:S(2)}) %collective-permute-start.28) | collective-permute-done | bytes 655392 | tf_op jit(solution)/shard_map/ppermute | solution.py:33
  213.2 0.9 copy-done.10
  214.1 5.6 %joined.2 = (f32[1024,2,1024]{2,1,0:T(2,128)}, f32[1024,1024]{1,0:T(8,128)}) custom-call(s32[1]{0:T(128)} %bitcast.21.place_ref, bf16[1024,1024]{1,0:T(8,128)(2,1)} %get-tuple-element.215.gate_ref, bf16[320,1024]{1,0:T(8,128)(2,1)} %get-tuple-element.171.first_ref.rest_0_, bf16[320,1024]{1,0:T(8,128)(2,1)} %copy-done.10, ...), custom_call_target="tpu_custom_call" | custom-call | flops 1 | bytes 1 | tf_op jit(solution)/shard_map/joined/pallas_call | solution.py:1034
  219.7 0.8 copy-done.9
  220.6 5.3 %joined.3 = (f32[1024,2,1024]{2,1,0:T(2,128)}, f32[64,1024]{1,0:T(8,128)}, f32[16,1024]{1,0:T(8,128)}, f32[1,1024]{1,0:T(1,128)}, f32[1,1024]{1,0:T(1,128)}, /*i...) custom-call(s32[1]{0:T(128)} %bitcast.21.place_ref, ...), custom_call_target="tpu_custom_call", output_to_operand_aliasing={{0}: (8, {})} | custom-call | flops 1 | bytes 1 | tf_op jit(solution)/shard_map/joined/pallas_call | solution.py:1034
  (130 shorter events, 9.8 us)
Async XLA Ops:
  7.2 206.0 %all-reduce.3.cloned.1.call-start = ((), (), s32[]{:S(2)}) async-start(), calls=%async_computation | async-start | bytes 8388608 | tf_op jit(solution)/shard_map/psum | solution.py:1217
  7.2 11.4 %collective-permute-start.19 = (bf16[256,512]{1,0:T(8,128)(2,1)}, bf16[256,512]{1,0:T(8,128)(2,1)S(1)}, u32[]{:S(2)}, u32[]{:S(2)}) collective-permute-start(bf16[256,512]{1,0:T(8,128)(2,1)} %own_ref.1), channel_id=1, source_target_pairs={{0,1},{1,0},{2,3},{3,2},{4,5},{5,4},{6,7},{7,6},{8,9},{9,8},{10,11... | collective-permute-start | bytes 786440 | tf_op jit(solution)/shard_map/ppermute | solution.py:33
  11.6 7.0 %collective-permute-start.21 = (bf16[16,512]{1,0:T(8,128)(2,1)}, bf16[16,512]{1,0:T(8,128)(2,1)S(1)}, u32[]{:S(2)}, u32[]{:S(2)}) collective-permute-start(bf16[16,512]{1,0:T(8,128)(2,1)} %edge_rows.1), channel_id=1, source_target_pairs={{0,3},{1,2},{2,5},{3,4},{4,7},{5,6},{6,9},{7,8},{8,11},{9,10},{10,... | collective-permute-start | bytes 49160 | tf_op jit(solution)/shard_map/ppermute | solution.py:51
  13.0 5.6 %collective-permute-start.20 = (bf16[16,512]{1,0:T(8,128)(2,1)}, bf16[16,512]{1,0:T(8,128)(2,1)S(1)}, u32[]{:S(2)}, u32[]{:S(2)}) collective-permute-start(bf16[16,512]{1,0:T(8,128)(2,1)} %edge_rows.1), channel_id=1, source_target_pairs={{0,2},{2,4},{4,6},{6,8},{8,10},{10,12},{12,14},{14,16},{16,18},{18... | collective-permute-start | bytes 49160 | tf_op jit(solution)/shard_map/ppermute | solution.py:28
  17.0 12.9 %collective-permute-start.23 = (bf16[256,512]{1,0:T(8,128)(2,1)}, bf16[256,512]{1,0:T(8,128)(2,1)S(1)}, u32[]{:S(2)}, u32[]{:S(2)}) collective-permute-start(bf16[256,512]{1,0:T(8,128)(2,1)} %param.27), channel_id=1, source_target_pairs={{0,1},{1,0},{2,3},{3,2},{4,5},{5,4},{6,7},{7,6},{8,9},{9,8},{10,11... | collective-permute-start | bytes 786440 | tf_op jit(solution)/shard_map/ppermute | solution.py:33
  21.8 4.0 %copy-start.21 = (bf16[96,1024]{1,0:T(8,128)(2,1)S(1)}, bf16[96,1024]{1,0:T(8,128)(2,1)}, u32[]{:S(2)}) copy-start(bf16[96,1024]{1,0:T(8,128)(2,1)} %select_ref.1) | copy-start | bytes 589828
  21.8 4.0 %copy-start.31 = (f32[4,1024]{1,0:T(4,128)S(1)}, f32[4,1024]{1,0:T(4,128)}, u32[]{:S(2)}) copy-start(f32[4,1024]{1,0:T(4,128)} %conv_weight_ref.1) | copy-start | bytes 49156
  21.8 8.1 %copy-start.17 = (bf16[256,512]{1,0:T(8,128)(2,1)S(1)}, bf16[256,512]{1,0:T(8,128)(2,1)}, u32[]{:S(2)}) copy-start(bf16[256,512]{1,0:T(8,128)(2,1)} %param.27) | copy-start | bytes 786436
  25.8 4.2 %copy-start = (bf16[1024,1024]{1,0:T(8,128)(2,1)S(1)}, bf16[1024,1024]{1,0:T(8,128)(2,1)}, u32[]{:S(2)}) copy-start(bf16[1024,1024]{1,0:T(8,128)(2,1)} %param.25) | copy-start | bytes 6291460
  28.9 4.6 %collective-permute-start.22 = (f32[96,256]{1,0:T(8,128)S(1)}, f32[96,256]{1,0:T(8,128)S(1)}, u32[]{:S(2)}, u32[]{:S(2)}) collective-permute-start(f32[96,256]{1,0:T(8,128)S(1)} %get-tuple-element.152.selected_ref), channel_id=1, source_target_pairs={{0,1},{1,0},{2,3},{3,2},{4,5},{5,4},{6,7},{7,6},{8,9},{9,8},{10,11... | collective-permute-start | bytes 294920 | tf_op jit(solution)/shard_map/ppermute | solution.py:33
  29.9 13.6 %copy-start.11 = (bf16[256,512]{1,0:T(8,128)(2,1)}, bf16[256,512]{1,0:T(8,128)(2,1)S(1)}, u32[]{:S(2)}) copy-start(bf16[256,512]{1,0:T(8,128)(2,1)S(1)} %get-tuple-element.232) | copy-start | bytes 786436
  29.9 13.6 %copy-start.12 = (bf16[256,512]{1,0:T(8,128)(2,1)}, bf16[256,512]{1,0:T(8,128)(2,1)S(1)}, u32[]{:S(2)}) copy-start(bf16[256,512]{1,0:T(8,128)(2,1)S(1)} %get-tuple-element.233) | copy-start | bytes 786436
  29.9 3.6 %copy-start.15 = (f32[16,1024]{1,0:T(8,128)S(1)}, f32[16,1024]{1,0:T(8,128)}, u32[]{:S(2)}) copy-start(f32[16,1024]{1,0:T(8,128)} %decay_log_ref.7) | copy-start | bytes 196612
  29.9 3.6 %copy-start.23 = (bf16[64,1024]{1,0:T(8,128)(2,1)S(1)}, bf16[64,1024]{1,0:T(8,128)(2,1)}, u32[]{:S(2)}) copy-start(bf16[64,1024]{1,0:T(8,128)(2,1)} %step_weight_ref.1) | copy-start | bytes 393220
  33.5 10.0 %copy-start.20 = (f32[96,256]{1,0:T(8,128)}, f32[96,256]{1,0:T(8,128)S(1)}, u32[]{:S(2)}) copy-start(f32[96,256]{1,0:T(8,128)S(1)} %collective-permute-done.22.other_ref) | copy-start | bytes 294916
  43.5 1.6 collective-permute-start.24
  47.4 5.1 %collective-permute-start.25 = (bf16[48,1024]{1,0:T(8,128)(2,1)}, bf16[48,1024]{1,0:T(8,128)(2,1)S(1)}, u32[]{:S(2)}, u32[]{:S(2)}) collective-permute-start(bf16[48,1024]{1,0:T(8,128)(2,1)} %get-tuple-element.157.own_ref), channel_id=1, source_target_pairs={{0,4},{2,6},{4,0},{6,2},{8,12},{10,14},{12,8},{14,10},{16,20},{18,... | collective-permute-start | bytes 294920 | tf_op jit(solution)/shard_map/ppermute | solution.py:33
  54.9 6.5 %collective-permute-start.26 = (bf16[16,1024]{1,0:T(8,128)(2,1)}, bf16[16,1024]{1,0:T(8,128)(2,1)S(1)}, u32[]{:S(2)}, u32[]{:S(2)}) collective-permute-start(bf16[16,1024]{1,0:T(8,128)(2,1)} %get-tuple-element.160), channel_id=1, source_target_pairs={{0,8},{2,10},{4,12},{6,14},{8,16},{10,18},{12,20},{14,22},{16,24},... | collective-permute-start | bytes 98312 | tf_op jit(solution)/shard_map/ppermute | solution.py:28
  59.5 12.2 %collective-permute-start.27 = (bf16[16,1024]{1,0:T(8,128)(2,1)}, bf16[16,1024]{1,0:T(8,128)(2,1)S(1)}, u32[]{:S(2)}, u32[]{:S(2)}) collective-permute-start(bf16[16,1024]{1,0:T(8,128)(2,1)} %get-tuple-element.162), channel_id=1, source_target_pairs={{8,0},{10,2},{12,4},{14,6},{16,8},{18,10},{20,12},{22,14},{24,16},... | collective-permute-start | bytes 98312 | tf_op jit(solution)/shard_map/ppermute | solution.py:28
  71.7 3.2 %copy-start.3 = (bf16[256,1024]{1,0:T(8,128)(2,1)S(1)}, bf16[256,1024]{1,0:T(8,128)(2,1)}, u32[]{:S(2)}) copy-start(bf16[256,1024]{1,0:T(8,128)(2,1)} %get-tuple-element.164) | copy-start | bytes 1572868
  71.7 3.2 %copy-start.24 = (bf16[256,1024]{1,0:T(8,128)(2,1)S(1)}, bf16[256,1024]{1,0:T(8,128)(2,1)}, u32[]{:S(2)}) copy-start(bf16[256,1024]{1,0:T(8,128)(2,1)} %get-tuple-element.165) | copy-start | bytes 1572868
  100.5 5.6 %copy-start.19 = (f32[256,1024]{1,0:T(8,128)S(1)}, f32[256,1024]{1,0:T(8,128)}, u32[]{:S(2)}) copy-start(f32[256,1024]{1,0:T(8,128)} %get-tuple-element.79.convolved_ref) | copy-start | bytes 3145732 | tf_op jit(solution)/shard_map/cond
  100.6 5.6 %copy-start.22 = (bf16[96,1024]{1,0:T(8,128)(2,1)S(1)}, bf16[96,1024]{1,0:T(8,128)(2,1)}, u32[]{:S(2)}) copy-start(bf16[96,1024]{1,0:T(8,128)(2,1)} %get-tuple-element.77.select_ref) | copy-start | bytes 589828 | tf_op jit(solution)/shard_map/cond
  100.6 5.6 %collective-permute-start = (f32[96,256]{1,0:T(8,128)}, f32[96,256]{1,0:T(8,128)}, u32[]{:S(2)}, u32[]{:S(2)}) collective-permute-start(f32[96,256]{1,0:T(8,128)} %get-tuple-element.76.select_grad_ref.refs_1_), channel_id=1, source_target_pairs={{0,1},{1,0},{2,3},{3,2},{4,5},{5,4},{6,7},{7,6},{8,9},{9,8},{10,11... | collective-permute-start | bytes 294920 | tf_op jit(solution)/shard_map/cond/branch_1_fun/ppermute | solution.py:33
  104.0 9.6 %collective-permute-start.4 = (bf16[256,256]{1,0:T(8,128)(2,1)}, bf16[256,256]{1,0:T(8,128)(2,1)}, u32[]{:S(2)}, u32[]{:S(2)}) collective-permute-start(bf16[256,256]{1,0:T(8,128)(2,1)} %get-tuple-element.221), channel_id=1, source_target_pairs={{0,6},{2,4},{4,2},{6,0},{8,14},{10,12},{12,10},{14,8},{16,22},{18,... | collective-permute-start | bytes 393224 | tf_op jit(solution)/shard_map/cond/branch_1_fun/ppermute | solution.py:33
  104.0 9.6 %collective-permute-start.3 = (bf16[256,256]{1,0:T(8,128)(2,1)}, bf16[256,256]{1,0:T(8,128)(2,1)}, u32[]{:S(2)}, u32[]{:S(2)}) collective-permute-start(bf16[256,256]{1,0:T(8,128)(2,1)} %get-tuple-element.222), channel_id=1, source_target_pairs={{0,2},{2,0},{4,6},{6,4},{8,10},{10,8},{12,14},{14,12},{16,18},{18,... | collective-permute-start | bytes 393224 | tf_op jit(solution)/shard_map/cond/branch_1_fun/ppermute | solution.py:33
  104.7 8.9 %collective-permute-start.2 = (bf16[256,256]{1,0:T(8,128)(2,1)}, bf16[256,256]{1,0:T(8,128)(2,1)}, u32[]{:S(2)}, u32[]{:S(2)}) collective-permute-start(bf16[256,256]{1,0:T(8,128)(2,1)} %get-tuple-element.223), channel_id=1, source_target_pairs={{0,4},{2,6},{4,0},{6,2},{8,12},{10,14},{12,8},{14,10},{16,20},{18,... | collective-permute-start | bytes 393224 | tf_op jit(solution)/shard_map/cond/branch_1_fun/ppermute | solution.py:33
  110.2 11.7 %copy-start.25 = (bf16[256,1024]{1,0:T(8,128)(2,1)S(1)}, bf16[256,1024]{1,0:T(8,128)(2,1)}, u32[]{:S(2)}) copy-start(bf16[256,1024]{1,0:T(8,128)(2,1)} %get-tuple-element.85) | copy-start | bytes 1572868 | tf_op jit(solution)/shard_map/cond
  110.2 11.7 %copy-start.34 = (f32[1024]{0:T(1024)S(1)}, f32[1024]{0:T(1024)}, u32[]{:S(2)}) copy-start(f32[1024]{0:T(1024)} %get-tuple-element.89) | copy-start | bytes 12292 | tf_op jit(solution)/shard_map/cond
  110.2 3.4 %collective-permute-start.1 = (f32[8,1024]{1,0:T(8,128)}, f32[8,1024]{1,0:T(8,128)S(1)}, u32[]{:S(2)}, u32[]{:S(2)}) collective-permute-start(f32[8,1024]{1,0:T(8,128)} %get-tuple-element.83), channel_id=1, source_target_pairs={{2,0},{4,2},{6,4},{8,6},{10,8},{12,10},{14,12},{16,14},{18,16},{20... | collective-permute-start | bytes 98312 | tf_op jit(solution)/shard_map/cond/branch_1_fun/ppermute | solution.py:28
  115.7 21.7 %collective-permute-start.5 = (bf16[256,1024]{1,0:T(8,128)(2,1)}, bf16[256,1024]{1,0:T(8,128)(2,1)S(1)}, u32[]{:S(2)}, u32[]{:S(2)}) collective-permute-start(bf16[256,1024]{1,0:T(8,128)(2,1)} %patched.1.wait_ref.own_ref), channel_id=1, source_target_pairs={{0,4},{2,6},{4,0},{6,2},{8,12},{10,14},{12,8},{14,10},{16,20},{18,... | collective-permute-start | bytes 1572872 | tf_op jit(solution)/shard_map/cond/branch_1_fun/ppermute | solution.py:33
  119.7 8.6 %collective-permute-start.8 = (bf16[128,1024]{1,0:T(8,128)(2,1)}, bf16[128,1024]{1,0:T(8,128)(2,1)S(1)}, u32[]{:S(2)}, u32[]{:S(2)}) collective-permute-start(bf16[128,1024]{1,0:T(8,128)(2,1)} %get-tuple-element.93), channel_id=1, source_target_pairs={{0,2},{2,0},{4,6},{6,4},{8,10},{10,8},{12,14},{14,12},{16,18},{18,... | collective-permute-start | bytes 786440 | tf_op jit(solution)/shard_map/cond/branch_1_fun/ppermute | solution.py:33
  126.2 17.0 %copy-start.5 = (f32[256,1024]{1,0:T(8,128)}, f32[256,1024]{1,0:T(8,128)S(1)}, u32[]{:S(2)}) copy-start(f32[256,1024]{1,0:T(8,128)S(1)} %get-tuple-element.231) | copy-start | bytes 3145732 | tf_op jit(solution)/shard_map/cond
  126.2 12.0 %copy-start.2 = (bf16[256,1024]{1,0:T(8,128)(2,1)S(1)}, bf16[256,1024]{1,0:T(8,128)(2,1)}, u32[]{:S(2)}) copy-start(bf16[256,1024]{1,0:T(8,128)(2,1)} %patched.1.wait_ref.own_ref) | copy-start | bytes 1572868 | tf_op jit(solution)/shard_map/cond
  126.2 5.0 %collective-permute-start.6 = (f32[1,1024]{1,0:T(1,128)S(1)}, f32[1,1024]{1,0:T(1,128)S(1)}, u32[]{:S(2)}, u32[]{:S(2)}) collective-permute-start(f32[1,1024]{1,0:T(1,128)S(1)} %bitcast.46), channel_id=1, source_target_pairs={{0,1},{1,0},{2,3},{3,2},{4,5},{5,4},{6,7},{7,6},{8,9},{9,8},{10,11... | collective-permute-start | bytes 12296 | tf_op jit(solution)/shard_map/cond/branch_1_fun/ppermute | solution.py:33
  127.2 4.6 %collective-permute-start.7 = (f32[1,256]{1,0:T(1,128)S(1)}, f32[1,256]{1,0:T(1,128)S(1)}, u32[]{:S(2)}, u32[]{:S(2)}) collective-permute-start(f32[1,256]{1,0:T(1,128)S(1)} %bitcast.50), channel_id=1, source_target_pairs={{0,1},{1,0},{2,3},{3,2},{4,5},{5,4},{6,7},{7,6},{8,9},{9,8},{10,11... | collective-permute-start | bytes 3080 | tf_op jit(solution)/shard_map/cond/branch_1_fun/ppermute | solution.py:33
  130.9 6.5 %collective-permute-start.9 = (bf16[64,1024]{1,0:T(8,128)(2,1)}, bf16[64,1024]{1,0:T(8,128)(2,1)S(1)}, u32[]{:S(2)}, u32[]{:S(2)}) collective-permute-start(bf16[64,1024]{1,0:T(8,128)(2,1)} %get-tuple-element.94), channel_id=1, source_target_pairs={{0,4},{2,6},{4,0},{6,2},{8,12},{10,14},{12,8},{14,10},{16,20},{18,... | collective-permute-start | bytes 393224 | tf_op jit(solution)/shard_map/cond/branch_1_fun/ppermute | solution.py:33
  131.8 5.6 %copy-start.37 = (f32[1,256]{1,0:T(1,128)}, f32[1,256]{1,0:T(1,128)S(1)}, u32[]{:S(2)}) copy-start(f32[1,256]{1,0:T(1,128)S(1)} %collective-permute-done.7.refs_2_) | copy-start | bytes 3076 | tf_op jit(solution)/shard_map/cond
  138.2 3.0 %copy-start.38 = (f32[1,256]{1,0:T(1,128)S(1)}, f32[1,256]{1,0:T(1,128)}, u32[]{:S(2)}) copy-start(f32[1,256]{1,0:T(1,128)} %copy-done.37) | copy-start | bytes 3076 | tf_op jit(solution)/shard_map/cond
  140.3 2.9 %collective-permute-start.10 = (bf16[512,1024]{1,0:T(8,128)(2,1)}, bf16[512,1024]{1,0:T(8,128)(2,1)S(1)}, u32[]{:S(2)}, u32[]{:S(2)}) collective-permute-start(bf16[512,1024]{1,0:T(8,128)(2,1)} %pad_maximum_fusion), channel_id=1, source_target_pairs={{0,2},{2,0},{4,6},{6,4},{8,10},{10,8},{12,14},{14,12},{16,18},{18,... | collective-permute-start | bytes 3145736 | tf_op jit(solution)/shard_map/cond/branch_1_fun/ppermute | solution.py:33
  143.2 1.0 copy-start.16
  147.6 0.9 copy-start.41
  147.6 3.4 %copy-start.40 = (bf16[80,1024]{1,0:T(8,128)(2,1)S(1)}, bf16[80,1024]{1,0:T(8,128)(2,1)}, u32[]{:S(2)}) copy-start(bf16[80,1024]{1,0:T(8,128)(2,1)} %get-tuple-element.98) | copy-start | bytes 491524 | tf_op jit(solution)/shard_map/cond
  147.6 5.9 %copy-start.39 = (bf16[80,1024]{1,0:T(8,128)(2,1)S(1)}, bf16[80,1024]{1,0:T(8,128)(2,1)}, u32[]{:S(2)}) copy-start(bf16[80,1024]{1,0:T(8,128)(2,1)} %get-tuple-element.99) | copy-start | bytes 491524 | tf_op jit(solution)/shard_map/cond
  147.6 5.9 %copy-start.1 = (bf16[1024,1024]{1,0:T(8,128)(2,1)S(1)}, bf16[1024,1024]{1,0:T(8,128)(2,1)}, u32[]{:S(2)}) copy-start(bf16[1024,1024]{1,0:T(8,128)(2,1)} %get-tuple-element.103) | copy-start | bytes 6291460 | tf_op jit(solution)/shard_map/cond
  147.7 19.1 %copy-start.7 = (f32[80,1024]{1,0:T(8,128)S(1)}, f32[80,1024]{1,0:T(8,128)}, u32[]{:S(2)}) copy-start(f32[80,1024]{1,0:T(8,128)} %get-tuple-element.96.refs_1_) | copy-start | bytes 983044 | tf_op jit(solution)/shard_map/cond
  148.5 12.9 %collective-permute-start.11 = (bf16[80,1024]{1,0:T(8,128)(2,1)S(1)}, bf16[80,1024]{1,0:T(8,128)(2,1)S(1)}, u32[]{:S(2)}, u32[]{:S(2)}) collective-permute-start(bf16[80,1024]{1,0:T(8,128)(2,1)S(1)} %copy-done.41), channel_id=1, source_target_pairs={{0,8},{2,10},{4,12},{6,14},{8,0},{10,2},{12,4},{14,6},{16,24},{18,... | collective-permute-start | bytes 491528 | tf_op jit(solution)/shard_map/cond/branch_1_fun/ppermute | solution.py:33
  151.0 10.5 %collective-permute-start.12 = (bf16[80,1024]{1,0:T(8,128)(2,1)S(1)}, bf16[80,1024]{1,0:T(8,128)(2,1)S(1)}, u32[]{:S(2)}, u32[]{:S(2)}) collective-permute-start(bf16[80,1024]{1,0:T(8,128)(2,1)S(1)} %copy-done.40), channel_id=1, source_target_pairs={{0,16},{2,18},{4,20},{6,22},{8,24},{10,26},{12,28},{14,30},{16,0},... | collective-permute-start | bytes 491528 | tf_op jit(solution)/shard_map/cond/branch_1_fun/ppermute | solution.py:33
  153.6 13.2 %collective-permute-start.13 = (bf16[80,1024]{1,0:T(8,128)(2,1)S(1)}, bf16[80,1024]{1,0:T(8,128)(2,1)S(1)}, u32[]{:S(2)}, u32[]{:S(2)}) collective-permute-start(bf16[80,1024]{1,0:T(8,128)(2,1)S(1)} %copy-done.39), channel_id=1, source_target_pairs={{0,24},{2,26},{4,28},{6,30},{8,16},{10,18},{12,20},{14,22},{16,8},... | collective-permute-start | bytes 491528 | tf_op jit(solution)/shard_map/cond/branch_1_fun/ppermute | solution.py:33
  154.3 19.4 %copy-start.14 = (f32[256,512]{1,0:T(8,128)S(1)}, f32[256,512]{1,0:T(8,128)}, u32[]{:S(2)}) copy-start(f32[256,512]{1,0:T(8,128)} %after.8) | copy-start | bytes 1572868 | tf_op jit(solution)/shard_map/cond
  166.9 15.8 %collective-permute-start.16 = (bf16[80,1024]{1,0:T(8,128)(2,1)S(1)}, bf16[80,1024]{1,0:T(8,128)(2,1)S(1)}, u32[]{:S(2)}, u32[]{:S(2)}) collective-permute-start(bf16[80,1024]{1,0:T(8,128)(2,1)S(1)} %pad_maximum_fusion.4), channel_id=1, source_target_pairs={{0,8},{2,10},{4,12},{6,14},{8,0},{10,2},{12,4},{14,6},{16,24},{18,... | collective-permute-start | bytes 491528 | tf_op jit(solution)/shard_map/cond/branch_1_fun/ppermute | solution.py:33
  172.4 25.5 %copy-start.6 = (f32[256,1024]{1,0:T(8,128)S(1)}, f32[256,1024]{1,0:T(8,128)}, u32[]{:S(2)}) copy-start(f32[256,1024]{1,0:T(8,128)} %copy-done.5) | copy-start | bytes 3145732 | tf_op jit(solution)/shard_map/cond
  172.4 25.5 %copy-start.13 = (bf16[256,512]{1,0:T(8,128)(2,1)S(1)}, bf16[256,512]{1,0:T(8,128)(2,1)}, u32[]{:S(2)}) copy-start(bf16[256,512]{1,0:T(8,128)(2,1)} %get-tuple-element.100) | copy-start | bytes 786436 | tf_op jit(solution)/shard_map/cond
  172.4 25.5 %copy-start.18 = (bf16[256,512]{1,0:T(8,128)(2,1)S(1)}, bf16[256,512]{1,0:T(8,128)(2,1)}, u32[]{:S(2)}) copy-start(bf16[256,512]{1,0:T(8,128)(2,1)} %get-tuple-element.104) | copy-start | bytes 786436 | tf_op jit(solution)/shard_map/cond
  172.5 25.4 %collective-permute-start.17 = (f32[256,512]{1,0:T(8,128)S(1)}, f32[256,512]{1,0:T(8,128)S(1)}, u32[]{:S(2)}, u32[]{:S(2)}) collective-permute-start(f32[256,512]{1,0:T(8,128)S(1)} %slice_select_fusion.1), channel_id=1, source_target_pairs={{0,1},{1,0},{2,3},{3,2},{4,5},{5,4},{6,7},{7,6},{8,9},{9,8},{10,11... | collective-permute-start | bytes 1572872 | tf_op jit(solution)/shard_map/cond/branch_1_fun/ppermute | solution.py:33
  173.7 24.2 %collective-permute-start.18 = (f32[256,512]{1,0:T(8,128)S(1)}, f32[256,512]{1,0:T(8,128)S(1)}, u32[]{:S(2)}, u32[]{:S(2)}) collective-permute-start(f32[256,512]{1,0:T(8,128)S(1)} %copy-done.14), channel_id=1, source_target_pairs={{0,1},{1,0},{2,3},{3,2},{4,5},{5,4},{6,7},{7,6},{8,9},{9,8},{10,11... | collective-permute-start | bytes 1572872 | tf_op jit(solution)/shard_map/cond/branch_1_fun/ppermute | solution.py:33
  174.5 15.6 %collective-permute-start.15 = (bf16[80,1024]{1,0:T(8,128)(2,1)S(1)}, bf16[80,1024]{1,0:T(8,128)(2,1)S(1)}, u32[]{:S(2)}, u32[]{:S(2)}) collective-permute-start(bf16[80,1024]{1,0:T(8,128)(2,1)S(1)} %pad_maximum_fusion.4), channel_id=1, source_target_pairs={{0,16},{2,18},{4,20},{6,22},{8,24},{10,26},{12,28},{14,30},{16,0},... | collective-permute-start | bytes 491528 | tf_op jit(solution)/shard_map/cond/branch_1_fun/ppermute | solution.py:33
  175.9 20.9 %collective-permute-start.14 = (bf16[80,1024]{1,0:T(8,128)(2,1)S(1)}, bf16[80,1024]{1,0:T(8,128)(2,1)S(1)}, u32[]{:S(2)}, u32[]{:S(2)}) collective-permute-start(bf16[80,1024]{1,0:T(8,128)(2,1)S(1)} %pad_maximum_fusion.4), channel_id=1, source_target_pairs={{0,24},{2,26},{4,28},{6,30},{8,16},{10,18},{12,20},{14,22},{16,8},... | collective-permute-start | bytes 491528 | tf_op jit(solution)/shard_map/cond/branch_1_fun/ppermute | solution.py:33
  199.0 14.2 %collective-permute-start.28 = (bf16[320,1024]{1,0:T(8,128)(2,1)}, bf16[320,1024]{1,0:T(8,128)(2,1)S(1)}, u32[]{:S(2)}, u32[]{:S(2)}) collective-permute-start(bf16[320,1024]{1,0:T(8,128)(2,1)} %get-tuple-element.171.first_ref.rest_0_), channel_id=1, source_target_pairs={{0,4},{2,6},{4,0},{6,2},{8,12},{10,14},{12,8},{14,10},{16,20},{18,... | collective-permute-start | bytes 1966088 | tf_op jit(solution)/shard_map/ppermute | solution.py:33
  200.1 13.1 %collective-permute-start.30 = (bf16[320,1024]{1,0:T(8,128)(2,1)}, bf16[320,1024]{1,0:T(8,128)(2,1)S(1)}, u32[]{:S(2)}, u32[]{:S(2)}) collective-permute-start(bf16[320,1024]{1,0:T(8,128)(2,1)} %get-tuple-element.171.first_ref.rest_0_), channel_id=1, source_target_pairs={{0,2},{2,0},{4,6},{6,4},{8,10},{10,8},{12,14},{14,12},{16,18},{18,... | collective-permute-start | bytes 1966088 | tf_op jit(solution)/shard_map/ppermute | solution.py:33
  213.2 6.5 %copy-start.8 = (bf16[320,1024]{1,0:T(8,128)(2,1)}, bf16[320,1024]{1,0:T(8,128)(2,1)S(1)}, u32[]{:S(2)}) copy-start(bf16[320,1024]{1,0:T(8,128)(2,1)S(1)} %collective-permute-done.28.first_ref.rest_2_) | copy-start | bytes 1966084
  213.2 6.5 %collective-permute-start.29 = (bf16[320,1024]{1,0:T(8,128)(2,1)S(1)}, bf16[320,1024]{1,0:T(8,128)(2,1)S(1)}, u32[]{:S(2)}, u32[]{:S(2)}) collective-permute-start(bf16[320,1024]{1,0:T(8,128)(2,1)S(1)} %collective-permute-done.28.first_ref.rest_2_), channel_id=1, source_target_pairs={{0,2},{2,0},{4,6},{6,4},{8,10},{10,8},{12,14},{14,12},{16,18},{18,... | collective-permute-start | bytes 1966088 | tf_op jit(solution)/shard_map/ppermute | solution.py:33
  213.2 0.9 copy-start.10
  219.7 0.8 copy-start.9
  (10 other events, 6.6 us)
Sparse Core Ops, SparseCore 0:
  77.1 133.3 all-reduce.2

commit v19 on v18

--- a/solution.py
+++ b/solution.py
@@ -371,8 +371,12 @@
     passed_ref,
     entering_ref,
     skip_ref,
+    cot_ref,
+    normed_ref,
     gated_ref,
     gate_grad_ref,
+    out_product_ref,
+    gate_product_ref,
     entry_ref,
     coef,
     held_step,
@@ -407,13 +411,33 @@
     gate = gate_ref[...].astype(f32)
     logistic = jax.nn.sigmoid(gate)
     total = scanned[...] + skip_ref[...] * act
-    gated_ref[...] = (total * (gate * logistic)).astype(bf16)
+    gated = (total * (gate * logistic)).astype(bf16)
+    gated_ref[...] = gated
+    out_product_ref[...] = lax.dot_general(
+        gated, cot_ref[...], contract_first, preferred_element_type=f32
+    ).astype(bf16)
     slope = logistic * (1.0 + gate * (1.0 - logistic))
-    gate_grad_ref[...] = (gated_grad_ref[...] * total * slope).astype(bf16)
+    gate_grad = (gated_grad_ref[...] * total * slope).astype(bf16)
+    gate_grad_ref[...] = gate_grad
+    gate_product_ref[...] = lax.dot_general(
+        normed_ref[...], gate_grad, contract_first, preferred_element_type=f32
+    ).astype(bf16)
 
 
 def scan_forward(
-    selected, other, step, act, projected, gated_grad, masks, decay_log, passed, entering, skip_gain
+    selected,
+    other,
+    step,
+    act,
+    projected,
+    gated_grad,
+    masks,
+    decay_log,
+    passed,
+    entering,
+    skip_gain,
+    cot,
+    normed,
 ):
     rows, width = step.shape
     count = decay_log.shape[0]
@@ -434,11 +458,21 @@
             column_spec(2 * count + 8),
             column_spec(count),
             column_spec(1),
+            whole_spec(*cot.shape),
+            whole_spec(*normed.shape),
         ],
-        [column_spec(rows), column_spec(rows), column_spec(count)],
+        [
+            column_spec(rows),
+            column_spec(rows),
+            pl.BlockSpec((scan_width, cot.shape[1]), lambda j: (j, 0)),
+            column_spec(normed.shape[1]),
+            column_spec(count),
+        ],
         [
             jax.ShapeDtypeStruct((rows, width), bf16),
             jax.ShapeDtypeStruct((rows, width), bf16),
+            jax.ShapeDtypeStruct((width, cot.shape[1]), bf16),
+            jax.ShapeDtypeStruct((normed.shape[1], width), bf16),
             jax.ShapeDtypeStruct((count, width), f32),
         ],
         [pltpu.VMEM((2 * count, rows), f32)]
@@ -455,6 +489,8 @@
         passed,
         entering,
         skip_gain,
+        cot,
+        normed,
     )
 
 
@@ -1196,7 +1232,7 @@
         decay_log,
     )
     passed, entering, returning = carried(ends, decay_log)
-    gated, gate_grad, entry = scan_forward(
+    gated, gate_grad, out_product, gate_product, entry = scan_forward(
         selected,
         other_selected,
         step,
@@ -1208,12 +1244,10 @@
         passed,
         entering,
         skip_gain[None],
-    )
-    gated = after(gated, returning)
-    products = (
-        lax.dot_general(gated, cot_whole, contract_first, preferred_element_type=f32).astype(bf16),
-        lax.dot_general(normed, gate_grad, contract_first, preferred_element_type=f32).astype(bf16),
-    )
+        cot_whole,
+        normed,
+    )
+    products = (after(out_product, returning), gate_product)
     out_sum, gate_sum = lax.psum(products, "wide")
     wide_place = lax.axis_index("wide").astype(jnp.int32)
     four_place = (wide_place & 3)[None]

time: 234 us -> 228 us (0.974)
  matrix products: 15 us -> 9.88 us
  local copies, waits for them, and re-layouts: 11.3 us -> 6.94 us
  waiting for transfers between devices: 61.3 us -> 64.8 us
    dot_general x2 -> x0, matrix products: 5.25 us -> none  [the longest x1 3.18 us: local(): lax.dot_general(gated, cot_whole, contract_first, preferred_element_type=...]
    ppermute x26, waiting for transfers between devices: 60.1 us -> 62.7 us  [swapped(): return lax.ppermute(array, axis, [(i, i ^ bit) for i in range(peers)])]
  transfers between devices with their start and end apart: 32 -> 32, of which waited for: 13 -> 15; matrix products, arithmetic and copies ran while one was open for 8% -> 8% of each run, Pallas kernels for 25% -> 26%
where the time goes in v19:
time: 228 us
  Pallas kernels  78.7 us (35%)
  waiting for transfers between devices  64.8 us (28%)
  starting transfers between devices  45.7 us (20%)
  between operations  14.3 us (6%)
  matrix products  9.88 us (4%)
  other arithmetic  7.12 us (3%)
  local copies, waits for them, and re-layouts  6.94 us (3%)
    ppermute x26, waiting for transfers between devices, swapped(): return lax.ppermute(array, axis, [(i, i ^ bit) for i in range(peers)])  62.7 us
    pallas_call x5, Pallas kernels, call(): pl.pallas_call(kernel, grid=(width // scan_width,), in_specs=in_specs, ou...  52 us
    ppermute x26, starting transfers between devices, swapped(): return lax.ppermute(array, axis, [(i, i ^ bit) for i in range(peers)])  32.6 us
    ppermute x4, starting transfers between devices, passed_along(): return lax.ppermute(array, axis, pairs)  11.7 us
    pallas_call x2, Pallas kernels, joined(): pl.pallas_call(kernel, grid_spec=pltpu.PrefetchScalarGridSpec(num_scalar_...  10.5 us
  transfers between devices with their start and end apart: 32, of which 15 were waited for; matrix products, arithmetic and copies ran while one was open for 8% of the time, Pallas kernels for 26%

profile of v19, /device:TPU:0, one launch (start us, length us, event | category | flops | bytes accessed | tf_op | source)
XLA Modules:
  0.0 227.7 jit_solution(4773188345790437494)
XLA Ops:
  7.2 3.0 %collective-permute-start.19 = (bf16[256,512]{1,0:T(8,128)(2,1)}, bf16[256,512]{1,0:T(8,128)(2,1)S(1)}, u32[]{:S(2)}, u32[]{:S(2)}) collective-permute-start(bf16[256,512]{1,0:T(8,128)(2,1)} %own_ref.1), channel_id=1, source_target_pairs={{0,1},{1,0},{2,3},{3,2},{4,5},{5,4},{6,7},{7,6},{8,9},{9,8},{10,11... | collective-permute-start | bytes 786440 | tf_op jit(solution)/shard_map/ppermute | solution.py:33
  10.3 1.4 edge_rows.1
  11.6 1.3 collective-permute-start.21
  13.0 4.0 %collective-permute-start.20 = (bf16[16,512]{1,0:T(8,128)(2,1)}, bf16[16,512]{1,0:T(8,128)(2,1)S(1)}, u32[]{:S(2)}, u32[]{:S(2)}) collective-permute-start(bf16[16,512]{1,0:T(8,128)(2,1)} %edge_rows.1), channel_id=1, source_target_pairs={{0,2},{2,4},{4,6},{6,8},{8,10},{10,12},{12,14},{14,16},{16,18},{18... | collective-permute-start | bytes 49160 | tf_op jit(solution)/shard_map/ppermute | solution.py:28
  17.0 1.6 collective-permute-start.23
  19.3 2.3 %normalized.1 = (bf16[256,1024]{1,0:T(8,128)(2,1)}, bf16[272,1024]{1,0:T(8,128)(2,1)}, bf16[256,1024]{1,0:T(8,128)(2,1)S(1)}, f32[256,1]{1,0:T(8,128)}, f32[256,128]{1,0:T(8,128)S(1)}) custom-call(bf16[256,512]{1,0:T(8,128)(2,1)} %own_ref.1, bf16[256,512]{1,0:T(8,128)(2,1)} %copy-done.27, bf16[16,512]{1,0:T(8,128)(2,1)} %copy-done.35, ...), custom_call_target="tpu_custom_call" | custom-call | flops 1 | bytes 1 | tf_op jit(solution)/shard_map/normalized/pallas_call | solution.py:819
  21.6 4.0 %fusion.25.inner_ref.gate_ref = bf16[2,272,1024]{2,1,0:T(8,128)(2,1)S(1)} fusion(bf16[1024,2,1024]{2,1,0:T(2,128)(2,1)} %param.17, bf16[272,1024]{1,0:T(8,128)(2,1)} %get-tuple-element.152), kind=kOutput, calls=%fused_computation.47 | convolution fusion | flops 1141407744 | bytes 5865472 | tf_op jit(solution)/shard_map/td,dce->cte/dot_general | solution.py:1212
  25.6 3.1 %convolve.1 = (f32[256,1024]{1,0:T(8,128)}, bf16[256,1024]{1,0:T(8,128)(2,1)S(1)}, f32[96,256]{1,0:T(8,128)S(1)}) custom-call(bf16[2,272,1024]{2,1,0:T(8,128)(2,1)S(1)} %fusion.25.inner_ref.gate_ref, f32[4,1024]{1,0:T(4,128)S(1)} %copy-done.30, f32[1,1024]{1,0:T(1,128)} %bitcast.40, bf16[96,1024]{1,0:T(8,128)(2,1)S(1)} %copy-done.21, ...), custom_call_target="tpu_custom_call" | custom-call | flops 1 | bytes 1 | tf_op jit(solution)/shard_map/convolve/pallas_call | solution.py:127
  28.7 0.9 collective-permute-start.22
  29.8 0.7 fusion.29.gated_grad_ref
  30.5 2.8 %collective-permute-done.22.other_ref = f32[96,256]{1,0:T(8,128)S(1)} collective-permute-done((f32[96,256]{1,0:T(8,128)S(1)}, f32[96,256]{1,0:T(8,128)S(1)}, u32[]{:S(2)}, u32[]{:S(2)}) %collective-permute-start.22) | collective-permute-done | bytes 98336 | tf_op jit(solution)/shard_map/ppermute | solution.py:33
  33.4 10.0 %scan_ends.1 = (f32[256,1024]{1,0:T(8,128)}, f32[256,1024]{1,0:T(8,128)}, bf16[48,1024]{1,0:T(8,128)(2,1)}) custom-call(f32[96,256]{1,0:T(8,128)S(1)} %get-tuple-element.154.selected_ref, f32[96,256]{1,0:T(8,128)S(1)} %collective-permute-done.22.other_ref, bf16[64,1024]{1,0:T(8,128)(2,1)S(1)} %copy-done.22, f32[1,1024]{1,0:T(1,128)} %bitcast.41, ...), custom_call_target="tpu_custom_call" | custom-call | flops 1 | bytes 1 | tf_op jit(solution)/shard_map/scan_ends/pallas_call | solution.py:127
  43.5 1.6 collective-permute-done.24.other_ref
  45.1 1.7 carry_round.2
  46.8 1.7 collective-permute-start.25
  48.5 3.5 %collective-permute-done.25.other_ref = bf16[48,1024]{1,0:T(8,128)(2,1)} collective-permute-done((bf16[48,1024]{1,0:T(8,128)(2,1)}, bf16[48,1024]{1,0:T(8,128)(2,1)}, u32[]{:S(2)}, u32[]{:S(2)}) %collective-permute-start.25) | collective-permute-done | bytes 98336 | tf_op jit(solution)/shard_map/ppermute | solution.py:33
  52.0 1.8 carry_round.3
  53.7 4.6 %collective-permute-start.26 = (bf16[16,1024]{1,0:T(8,128)(2,1)}, bf16[16,1024]{1,0:T(8,128)(2,1)S(1)}, u32[]{:S(2)}, u32[]{:S(2)}) collective-permute-start(bf16[16,1024]{1,0:T(8,128)(2,1)} %get-tuple-element.162), channel_id=1, source_target_pairs={{0,8},{2,10},{4,12},{6,14},{8,16},{10,18},{12,20},{14,22},{16,24},... | collective-permute-start | bytes 98312 | tf_op jit(solution)/shard_map/ppermute | solution.py:28
  58.3 1.5 collective-permute-start.27
  59.8 1.9 pad_maximum_fusion.5.cot_ref
  62.4 11.3 %scan_forward.1 = (bf16[256,1024]{1,0:T(8,128)(2,1)}, bf16[256,1024]{1,0:T(8,128)(2,1)}, bf16[1024,1024]{1,0:T(8,128)(2,1)}, bf16[1024,1024]{1,0:T(8,128)(2,1)}, f32[16,1024]{1,0:T(8,128)}) custom-call(f32[96,256]{1,0:T(8,128)S(1)} %get-tuple-element.154.selected_ref, f32[96,256]{1,0:T(8,128)} %copy-done.20, f32[256,1024]{1,0:T(8,128)} %get-tuple-element.157.step_ref, ...), custom_call_target="tpu_custom_call" | custom-call | flops 1 | bytes 1 | tf_op jit(solution)/shard_map/scan_forward/pallas_call | solution.py:127
  73.7 119.7 %conditional.1 = (bf16[320,1024]{1,0:T(8,128)(2,1)S(1)}, bf16[256,512]{1,0:T(8,128)(2,1)}, bf16[256,512]{1,0:T(8,128)(2,1)}) conditional(s32[]{:T(128)} %convert_element_type.43, () %tuple.16, (s32[]{:T(128)}, f32[1024]{0:T(1024)}, f32[96,256]{1,0:T(8,128)S(1)}, f32[96,256]{1,0:T(8,128)}, f32[256,1024]{1,0:T(8,128)}, ...), branch_computations={%region_0.1_spmd, %region_1.4_spmd} | conditional | flops 1621776640 | bytes 85911368 | solution.py:1343
  73.7 23.5 %scan_backward.1 = (f32[256,1024]{1,0:T(8,128)}, f32[96,256]{1,0:T(8,128)}, f32[82,1024]{1,0:T(8,128)}) custom-call(f32[96,256]{1,0:T(8,128)S(1)} %get-tuple-element.62.selected_ref, f32[96,256]{1,0:T(8,128)} %get-tuple-element.63.other_ref, f32[256,1024]{1,0:T(8,128)} %get-tuple-element.64.step_pre_ref, f32[256,1024]{1,0:T(8,128)} %get-tuple-element.65.step_ref, ...), custom_call_target="tpu_custom_call" | custom-call | flops 1 | bytes 1 | tf_op jit(solution)/shard_map/cond/branch_1_fun/scan_backward/pallas_call | solution.py:127
  97.3 1.5 collective-permute-start
  98.8 0.8 constant_dynamic-slice_fusion
  99.6 0.7 collective-permute-start.3
  100.3 1.4 collective-permute-start.2
  102.3 4.0 %convolve_grad.1 = (bf16[256,1024]{1,0:T(8,128)(2,1)}, f32[8,1024]{1,0:T(8,128)}, f32[8,1024]{1,0:T(8,128)}, f32[101,1024]{1,0:T(8,128)}) custom-call(f32[96,256]{1,0:T(8,128)} %get-tuple-element.76.select_grad_ref.refs_1_, f32[96,256]{1,0:T(8,128)} %collective-permute-done.other_ref, bf16[96,1024]{1,0:T(8,128)(2,1)} %get-tuple-element.77.select_ref, ...), custom_call_target="tpu_custom_call" | custom-call | flops 1 | bytes 1 | tf_op jit(solution)/shard_map/cond/branch_1_fun/convolve_grad/pallas_call | solution.py:127
  106.3 1.6 collective-permute-start.1
  108.0 1.7 collective-permute-done.1.next_ref
  110.6 1.4 patched.1.wait_ref.own_ref
  112.0 1.2 collective-permute-start.5
  113.2 2.2 small_halves.1
  115.5 3.0 %collective-permute-start.8 = (bf16[128,1024]{1,0:T(8,128)(2,1)}, bf16[128,1024]{1,0:T(8,128)(2,1)S(1)}, u32[]{:S(2)}, u32[]{:S(2)}) collective-permute-start(bf16[128,1024]{1,0:T(8,128)(2,1)} %get-tuple-element.93), channel_id=1, source_target_pairs={{0,2},{2,0},{4,6},{6,4},{8,10},{10,8},{12,14},{14,12},{16,18},{18,... | collective-permute-start | bytes 786440 | tf_op jit(solution)/shard_map/cond/branch_1_fun/ppermute | solution.py:33
  118.5 4.5 %fusion.7 = (f32[256]{0:T(256)S(1)}, f32[1024]{0:T(1024)S(1)}, f32[256,1024]{1,0:T(8,128)S(1)}) fusion(bf16[256,1024]{1,0:T(8,128)(2,1)} %get-tuple-element.87, f32[1024]{0:T(1024)S(1)} %copy-done.33, f32[256]{0:T(256)S(1)} %bitcast.38, bf16[1024,2,1024]{2,1,0:T(2,128)(2,1)} %get-tuple-element.208, bf16[1,256,1024]{2,1,0:T(8,128)(2,1)} %bitcast.48, ...), kind=kOutput, calls=%fused_computation.7 | convolution fusion | flops 1076099840 | bytes 6825984 | tf_op jit(solution)/shard_map/cond/branch_1_fun/cte,dce->td/dot_general | solution.py:1296
  123.0 1.5 collective-permute-start.6
  125.1 0.7 copy-done.28
  125.8 1.9 folded.1
  128.5 5.2 %collective-permute-done.9.refs_3_.arrived_ref = bf16[64,1024]{1,0:T(8,128)(2,1)S(1)} collective-permute-done((bf16[64,1024]{1,0:T(8,128)(2,1)}, bf16[64,1024]{1,0:T(8,128)(2,1)S(1)}, u32[]{:S(2)}, u32[]{:S(2)}) %collective-permute-start.9) | collective-permute-done | bytes 131104 | tf_op jit(solution)/shard_map/cond/branch_1_fun/ppermute | solution.py:33
  133.7 0.7 copy-done.26
  134.5 2.1 pad_maximum_fusion
  136.6 0.9 slice_select_fusion.refs_0_
  137.5 2.0 collective-permute-done.10.far_ref
  139.5 1.0 copy-done.16
  140.5 3.6 %inner_quarter.1 = (f32[80,1024]{1,0:T(8,128)}, bf16[80,1024]{1,0:T(8,128)(2,1)}, bf16[80,1024]{1,0:T(8,128)(2,1)}, bf16[80,1024]{1,0:T(8,128)(2,1)}) custom-call(s32[1]{0:T(128)} %bitcast.place_ref, bf16[256,1024]{1,0:T(8,128)(2,1)} %patched.1.wait_ref.own_ref, bf16[256,1024]{1,0:T(8,128)(2,1)} %after.6.near_ref, bf16[512,1024]{1,0:T(8,128)(2,1)} %copy-done.16, ...), custom_call_target="tpu_custom_call" | custom-call | flops 1 | bytes 1 | tf_op jit(solution)/shard_map/cond/branch_1_fun/inner_quarter/pallas_call | solution.py:1000
  144.1 2.7 %collective-permute-start.11 = (bf16[80,1024]{1,0:T(8,128)(2,1)}, bf16[80,1024]{1,0:T(8,128)(2,1)S(1)}, u32[]{:S(2)}, u32[]{:S(2)}) collective-permute-start(bf16[80,1024]{1,0:T(8,128)(2,1)} %get-tuple-element.97), channel_id=1, source_target_pairs={{0,8},{2,10},{4,12},{6,14},{8,0},{10,2},{12,4},{14,6},{16,24},{18,... | collective-permute-start | bytes 491528 | tf_op jit(solution)/shard_map/cond/branch_1_fun/ppermute | solution.py:33
  146.8 2.8 %collective-permute-start.12 = (bf16[80,1024]{1,0:T(8,128)(2,1)S(1)}, bf16[80,1024]{1,0:T(8,128)(2,1)S(1)}, u32[]{:S(2)}, u32[]{:S(2)}) collective-permute-start(bf16[80,1024]{1,0:T(8,128)(2,1)S(1)} %copy-done.40), channel_id=1, source_target_pairs={{0,16},{2,18},{4,20},{6,22},{8,24},{10,26},{12,28},{14,30},{16,0},... | collective-permute-start | bytes 491528 | tf_op jit(solution)/shard_map/cond/branch_1_fun/ppermute | solution.py:33
  150.0 0.7 fusion.30
  150.7 7.8 %collective-permute-done.11 = bf16[80,1024]{1,0:T(8,128)(2,1)S(1)} collective-permute-done((bf16[80,1024]{1,0:T(8,128)(2,1)}, bf16[80,1024]{1,0:T(8,128)(2,1)S(1)}, u32[]{:S(2)}, u32[]{:S(2)}) %collective-permute-start.11) | collective-permute-done | bytes 163872 | tf_op jit(solution)/shard_map/cond/branch_1_fun/ppermute | solution.py:33
  158.5 5.1 %collective-permute-done.12 = bf16[80,1024]{1,0:T(8,128)(2,1)S(1)} collective-permute-done((bf16[80,1024]{1,0:T(8,128)(2,1)S(1)}, bf16[80,1024]{1,0:T(8,128)(2,1)S(1)}, u32[]{:S(2)}, u32[]{:S(2)}) %collective-permute-start.12) | collective-permute-done | bytes 163872 | tf_op jit(solution)/shard_map/cond/branch_1_fun/ppermute | solution.py:33
  163.7 3.8 %collective-permute-start.16 = (bf16[80,1024]{1,0:T(8,128)(2,1)S(1)}, bf16[80,1024]{1,0:T(8,128)(2,1)S(1)}, u32[]{:S(2)}, u32[]{:S(2)}) collective-permute-start(bf16[80,1024]{1,0:T(8,128)(2,1)S(1)} %pad_maximum_fusion.4), channel_id=1, source_target_pairs={{0,8},{2,10},{4,12},{6,14},{8,0},{10,2},{12,4},{14,6},{16,24},{18,... | collective-permute-start | bytes 491528 | tf_op jit(solution)/shard_map/cond/branch_1_fun/ppermute | solution.py:33
  167.6 1.4 collective-permute-start.17
  169.0 0.7 collective-permute-start.18
  169.7 0.7 collective-permute-start.15
  170.4 1.7 collective-permute-start.14
  172.1 6.1 %collective-permute-done.16 = bf16[80,1024]{1,0:T(8,128)(2,1)S(1)} collective-permute-done((bf16[80,1024]{1,0:T(8,128)(2,1)S(1)}, bf16[80,1024]{1,0:T(8,128)(2,1)S(1)}, u32[]{:S(2)}, u32[]{:S(2)}) %collective-permute-start.16) | collective-permute-done | bytes 163872 | tf_op jit(solution)/shard_map/cond/branch_1_fun/ppermute | solution.py:33
  178.3 6.1 %collective-permute-done.15 = bf16[80,1024]{1,0:T(8,128)(2,1)S(1)} collective-permute-done((bf16[80,1024]{1,0:T(8,128)(2,1)S(1)}, bf16[80,1024]{1,0:T(8,128)(2,1)S(1)}, u32[]{:S(2)}, u32[]{:S(2)}) %collective-permute-start.15) | collective-permute-done | bytes 163872 | tf_op jit(solution)/shard_map/cond/branch_1_fun/ppermute | solution.py:33
  184.4 7.3 %collective-permute-done.14 = bf16[80,1024]{1,0:T(8,128)(2,1)S(1)} collective-permute-done((bf16[80,1024]{1,0:T(8,128)(2,1)S(1)}, bf16[80,1024]{1,0:T(8,128)(2,1)S(1)}, u32[]{:S(2)}, u32[]{:S(2)}) %collective-permute-start.14) | collective-permute-done | bytes 163872 | tf_op jit(solution)/shard_map/cond/branch_1_fun/ppermute | solution.py:33
  192.3 1.0 fusion.15
  193.4 0.8 collective-permute-start.28
  194.2 14.4 %collective-permute-done.28.first_ref.rest_2_ = bf16[320,1024]{1,0:T(8,128)(2,1)S(1)} collective-permute-done((bf16[320,1024]{1,0:T(8,128)(2,1)S(1)}, bf16[320,1024]{1,0:T(8,128)(2,1)S(1)}, u32[]{:S(2)}, u32[]{:S(2)}) %collective-permute-start.28) | collective-permute-done | bytes 655392 | tf_op jit(solution)/shard_map/ppermute | solution.py:33
  209.5 5.4 %joined.2 = (f32[1024,2,1024]{2,1,0:T(2,128)}, f32[1024,1024]{1,0:T(8,128)}) custom-call(s32[1]{0:T(128)} %bitcast.21.place_ref, bf16[1024,1024]{1,0:T(8,128)(2,1)} %get-tuple-element.219.gate_ref, bf16[320,1024]{1,0:T(8,128)(2,1)S(1)} %get-tuple-element.174.first_ref.rest_0_, bf16[320,1024]{1,0:T(8,128)(2,1)} %copy-done.9, ...), custom_call_target="tpu_custom_call" | custom-call | flops 1 | bytes 1 | tf_op jit(solution)/shard_map/joined/pallas_call | solution.py:1070
  215.0 0.8 copy-done.8
  215.8 5.0 %joined.3 = (f32[1024,2,1024]{2,1,0:T(2,128)}, f32[64,1024]{1,0:T(8,128)}, f32[16,1024]{1,0:T(8,128)}, f32[1,1024]{1,0:T(1,128)}, f32[1,1024]{1,0:T(1,128)}, /*i...) custom-call(s32[1]{0:T(128)} %bitcast.21.place_ref, ...), custom_call_target="tpu_custom_call", output_to_operand_aliasing={{0}: (8, {})} | custom-call | flops 1 | bytes 1 | tf_op jit(solution)/shard_map/joined/pallas_call | solution.py:1070
  (127 shorter events, 6.7 us)
Async XLA Ops:
  7.2 201.9 %all-reduce.3.cloned.1.call-start = ((), (), s32[]{:S(2)}) async-start(), calls=%async_computation | async-start | bytes 8388608 | tf_op jit(solution)/shard_map/psum | solution.py:1251
  7.2 11.4 %collective-permute-start.19 = (bf16[256,512]{1,0:T(8,128)(2,1)}, bf16[256,512]{1,0:T(8,128)(2,1)S(1)}, u32[]{:S(2)}, u32[]{:S(2)}) collective-permute-start(bf16[256,512]{1,0:T(8,128)(2,1)} %own_ref.1), channel_id=1, source_target_pairs={{0,1},{1,0},{2,3},{3,2},{4,5},{5,4},{6,7},{7,6},{8,9},{9,8},{10,11... | collective-permute-start | bytes 786440 | tf_op jit(solution)/shard_map/ppermute | solution.py:33
  11.6 7.0 %collective-permute-start.21 = (bf16[16,512]{1,0:T(8,128)(2,1)}, bf16[16,512]{1,0:T(8,128)(2,1)S(1)}, u32[]{:S(2)}, u32[]{:S(2)}) collective-permute-start(bf16[16,512]{1,0:T(8,128)(2,1)} %edge_rows.1), channel_id=1, source_target_pairs={{0,3},{1,2},{2,5},{3,4},{4,7},{5,6},{6,9},{7,8},{8,11},{9,10},{10,... | collective-permute-start | bytes 49160 | tf_op jit(solution)/shard_map/ppermute | solution.py:51
  13.0 5.6 %collective-permute-start.20 = (bf16[16,512]{1,0:T(8,128)(2,1)}, bf16[16,512]{1,0:T(8,128)(2,1)S(1)}, u32[]{:S(2)}, u32[]{:S(2)}) collective-permute-start(bf16[16,512]{1,0:T(8,128)(2,1)} %edge_rows.1), channel_id=1, source_target_pairs={{0,2},{2,4},{4,6},{6,8},{8,10},{10,12},{12,14},{14,16},{16,18},{18... | collective-permute-start | bytes 49160 | tf_op jit(solution)/shard_map/ppermute | solution.py:28
  17.0 12.7 %collective-permute-start.23 = (bf16[256,512]{1,0:T(8,128)(2,1)}, bf16[256,512]{1,0:T(8,128)(2,1)S(1)}, u32[]{:S(2)}, u32[]{:S(2)}) collective-permute-start(bf16[256,512]{1,0:T(8,128)(2,1)} %param.27), channel_id=1, source_target_pairs={{0,1},{1,0},{2,3},{3,2},{4,5},{5,4},{6,7},{7,6},{8,9},{9,8},{10,11... | collective-permute-start | bytes 786440 | tf_op jit(solution)/shard_map/ppermute | solution.py:33
  21.6 4.0 %copy-start.21 = (bf16[96,1024]{1,0:T(8,128)(2,1)S(1)}, bf16[96,1024]{1,0:T(8,128)(2,1)}, u32[]{:S(2)}) copy-start(bf16[96,1024]{1,0:T(8,128)(2,1)} %select_ref.1) | copy-start | bytes 589828
  21.6 4.0 %copy-start.30 = (f32[4,1024]{1,0:T(4,128)S(1)}, f32[4,1024]{1,0:T(4,128)}, u32[]{:S(2)}) copy-start(f32[4,1024]{1,0:T(4,128)} %conv_weight_ref.1) | copy-start | bytes 49156
  21.6 8.1 %copy-start.17 = (bf16[256,512]{1,0:T(8,128)(2,1)S(1)}, bf16[256,512]{1,0:T(8,128)(2,1)}, u32[]{:S(2)}) copy-start(bf16[256,512]{1,0:T(8,128)(2,1)} %param.27) | copy-start | bytes 786436
  25.6 4.2 %copy-start = (bf16[1024,1024]{1,0:T(8,128)(2,1)S(1)}, bf16[1024,1024]{1,0:T(8,128)(2,1)}, u32[]{:S(2)}) copy-start(bf16[1024,1024]{1,0:T(8,128)(2,1)} %param.25) | copy-start | bytes 6291460
  28.7 4.6 %collective-permute-start.22 = (f32[96,256]{1,0:T(8,128)S(1)}, f32[96,256]{1,0:T(8,128)S(1)}, u32[]{:S(2)}, u32[]{:S(2)}) collective-permute-start(f32[96,256]{1,0:T(8,128)S(1)} %get-tuple-element.154.selected_ref), channel_id=1, source_target_pairs={{0,1},{1,0},{2,3},{3,2},{4,5},{5,4},{6,7},{7,6},{8,9},{9,8},{10,11... | collective-permute-start | bytes 294920 | tf_op jit(solution)/shard_map/ppermute | solution.py:33
  29.7 13.6 %copy-start.10 = (bf16[256,512]{1,0:T(8,128)(2,1)}, bf16[256,512]{1,0:T(8,128)(2,1)S(1)}, u32[]{:S(2)}) copy-start(bf16[256,512]{1,0:T(8,128)(2,1)S(1)} %get-tuple-element.236) | copy-start | bytes 786436
  29.7 13.6 %copy-start.11 = (bf16[256,512]{1,0:T(8,128)(2,1)}, bf16[256,512]{1,0:T(8,128)(2,1)S(1)}, u32[]{:S(2)}) copy-start(bf16[256,512]{1,0:T(8,128)(2,1)S(1)} %get-tuple-element.237) | copy-start | bytes 786436
  29.7 3.6 %copy-start.15 = (f32[16,1024]{1,0:T(8,128)S(1)}, f32[16,1024]{1,0:T(8,128)}, u32[]{:S(2)}) copy-start(f32[16,1024]{1,0:T(8,128)} %decay_log_ref.7) | copy-start | bytes 196612
  29.8 3.6 %copy-start.22 = (bf16[64,1024]{1,0:T(8,128)(2,1)S(1)}, bf16[64,1024]{1,0:T(8,128)(2,1)}, u32[]{:S(2)}) copy-start(bf16[64,1024]{1,0:T(8,128)(2,1)} %step_weight_ref.1) | copy-start | bytes 393220
  33.4 10.0 %copy-start.20 = (f32[96,256]{1,0:T(8,128)}, f32[96,256]{1,0:T(8,128)S(1)}, u32[]{:S(2)}) copy-start(f32[96,256]{1,0:T(8,128)S(1)} %collective-permute-done.22.other_ref) | copy-start | bytes 294916
  43.4 1.7 collective-permute-start.24
  46.8 5.2 %collective-permute-start.25 = (bf16[48,1024]{1,0:T(8,128)(2,1)}, bf16[48,1024]{1,0:T(8,128)(2,1)}, u32[]{:S(2)}, u32[]{:S(2)}) collective-permute-start(bf16[48,1024]{1,0:T(8,128)(2,1)} %get-tuple-element.159.own_ref), channel_id=1, source_target_pairs={{0,4},{2,6},{4,0},{6,2},{8,12},{10,14},{12,8},{14,10},{16,20},{18,... | collective-permute-start | bytes 294920 | tf_op jit(solution)/shard_map/ppermute | solution.py:33
  53.7 8.0 %collective-permute-start.26 = (bf16[16,1024]{1,0:T(8,128)(2,1)}, bf16[16,1024]{1,0:T(8,128)(2,1)S(1)}, u32[]{:S(2)}, u32[]{:S(2)}) collective-permute-start(bf16[16,1024]{1,0:T(8,128)(2,1)} %get-tuple-element.162), channel_id=1, source_target_pairs={{0,8},{2,10},{4,12},{6,14},{8,16},{10,18},{12,20},{14,22},{16,24},... | collective-permute-start | bytes 98312 | tf_op jit(solution)/shard_map/ppermute | solution.py:28
  58.3 15.3 %collective-permute-start.27 = (bf16[16,1024]{1,0:T(8,128)(2,1)}, bf16[16,1024]{1,0:T(8,128)(2,1)S(1)}, u32[]{:S(2)}, u32[]{:S(2)}) collective-permute-start(bf16[16,1024]{1,0:T(8,128)(2,1)} %get-tuple-element.165), channel_id=1, source_target_pairs={{8,0},{10,2},{12,4},{14,6},{16,8},{18,10},{20,12},{22,14},{24,16},... | collective-permute-start | bytes 98312 | tf_op jit(solution)/shard_map/ppermute | solution.py:28
  97.2 5.0 %copy-start.19 = (f32[256,1024]{1,0:T(8,128)S(1)}, f32[256,1024]{1,0:T(8,128)}, u32[]{:S(2)}) copy-start(f32[256,1024]{1,0:T(8,128)} %get-tuple-element.79.convolved_ref) | copy-start | bytes 3145732 | tf_op jit(solution)/shard_map/cond
  97.3 5.0 %collective-permute-start = (f32[96,256]{1,0:T(8,128)}, f32[96,256]{1,0:T(8,128)}, u32[]{:S(2)}, u32[]{:S(2)}) collective-permute-start(f32[96,256]{1,0:T(8,128)} %get-tuple-element.76.select_grad_ref.refs_1_), channel_id=1, source_target_pairs={{0,1},{1,0},{2,3},{3,2},{4,5},{5,4},{6,7},{7,6},{8,9},{9,8},{10,11... | collective-permute-start | bytes 294920 | tf_op jit(solution)/shard_map/cond/branch_1_fun/ppermute | solution.py:33
  99.6 10.1 %collective-permute-start.4 = (bf16[256,256]{1,0:T(8,128)(2,1)}, bf16[256,256]{1,0:T(8,128)(2,1)S(1)}, u32[]{:S(2)}, u32[]{:S(2)}) collective-permute-start(bf16[256,256]{1,0:T(8,128)(2,1)} %get-tuple-element.225), channel_id=1, source_target_pairs={{0,6},{2,4},{4,2},{6,0},{8,14},{10,12},{12,10},{14,8},{16,22},{18,... | collective-permute-start | bytes 393224 | tf_op jit(solution)/shard_map/cond/branch_1_fun/ppermute | solution.py:33
  99.6 10.1 %collective-permute-start.3 = (bf16[256,256]{1,0:T(8,128)(2,1)}, bf16[256,256]{1,0:T(8,128)(2,1)S(1)}, u32[]{:S(2)}, u32[]{:S(2)}) collective-permute-start(bf16[256,256]{1,0:T(8,128)(2,1)} %get-tuple-element.226), channel_id=1, source_target_pairs={{0,2},{2,0},{4,6},{6,4},{8,10},{10,8},{12,14},{14,12},{16,18},{18,... | collective-permute-start | bytes 393224 | tf_op jit(solution)/shard_map/cond/branch_1_fun/ppermute | solution.py:33
  100.3 9.5 %collective-permute-start.2 = (bf16[256,256]{1,0:T(8,128)(2,1)}, bf16[256,256]{1,0:T(8,128)(2,1)S(1)}, u32[]{:S(2)}, u32[]{:S(2)}) collective-permute-start(bf16[256,256]{1,0:T(8,128)(2,1)} %get-tuple-element.227), channel_id=1, source_target_pairs={{0,4},{2,6},{4,0},{6,2},{8,12},{10,14},{12,8},{14,10},{16,20},{18,... | collective-permute-start | bytes 393224 | tf_op jit(solution)/shard_map/cond/branch_1_fun/ppermute | solution.py:33
  102.3 5.7 %copy-start.29 = (f32[256,1]{1,0:T(8,128)S(1)}, f32[256,1]{1,0:T(8,128)}, u32[]{:S(2)}) copy-start(f32[256,1]{1,0:T(8,128)} %get-tuple-element.210) | copy-start | bytes 3076 | tf_op jit(solution)/shard_map/cond
  102.3 8.3 %copy-start.36 = (s32[256]{0:T(256)S(1)}, s32[256]{0:T(256)}, u32[]{:S(2)}) copy-start(s32[256]{0:T(256)} %get-tuple-element.61.ids_ref) | copy-start | bytes 3076 | tf_op jit(solution)/shard_map/cond
  106.3 12.2 %copy-start.33 = (f32[1024]{0:T(1024)S(1)}, f32[1024]{0:T(1024)}, u32[]{:S(2)}) copy-start(f32[1024]{0:T(1024)} %get-tuple-element.89) | copy-start | bytes 12292 | tf_op jit(solution)/shard_map/cond
  106.3 3.4 %collective-permute-start.1 = (f32[8,1024]{1,0:T(8,128)}, f32[8,1024]{1,0:T(8,128)S(1)}, u32[]{:S(2)}, u32[]{:S(2)}) collective-permute-start(f32[8,1024]{1,0:T(8,128)} %get-tuple-element.83), channel_id=1, source_target_pairs={{2,0},{4,2},{6,4},{8,6},{10,8},{12,10},{14,12},{16,14},{18,16},{20... | collective-permute-start | bytes 98312 | tf_op jit(solution)/shard_map/cond/branch_1_fun/ppermute | solution.py:28
  109.8 0.8 copy-start.25
  112.0 21.7 %collective-permute-start.5 = (bf16[256,1024]{1,0:T(8,128)(2,1)}, bf16[256,1024]{1,0:T(8,128)(2,1)S(1)}, u32[]{:S(2)}, u32[]{:S(2)}) collective-permute-start(bf16[256,1024]{1,0:T(8,128)(2,1)} %patched.1.wait_ref.own_ref), channel_id=1, source_target_pairs={{0,4},{2,6},{4,0},{6,2},{8,12},{10,14},{12,8},{14,10},{16,20},{18,... | collective-permute-start | bytes 1572872 | tf_op jit(solution)/shard_map/cond/branch_1_fun/ppermute | solution.py:33
  115.5 9.6 %collective-permute-start.8 = (bf16[128,1024]{1,0:T(8,128)(2,1)}, bf16[128,1024]{1,0:T(8,128)(2,1)S(1)}, u32[]{:S(2)}, u32[]{:S(2)}) collective-permute-start(bf16[128,1024]{1,0:T(8,128)(2,1)} %get-tuple-element.93), channel_id=1, source_target_pairs={{0,2},{2,0},{4,6},{6,4},{8,10},{10,8},{12,14},{14,12},{16,18},{18,... | collective-permute-start | bytes 786440 | tf_op jit(solution)/shard_map/cond/branch_1_fun/ppermute | solution.py:33
  123.0 16.5 %copy-start.4 = (f32[256,1024]{1,0:T(8,128)}, f32[256,1024]{1,0:T(8,128)S(1)}, u32[]{:S(2)}) copy-start(f32[256,1024]{1,0:T(8,128)S(1)} %get-tuple-element.235) | copy-start | bytes 3145732 | tf_op jit(solution)/shard_map/cond
  123.0 11.5 %copy-start.2 = (bf16[256,1024]{1,0:T(8,128)(2,1)S(1)}, bf16[256,1024]{1,0:T(8,128)(2,1)}, u32[]{:S(2)}) copy-start(bf16[256,1024]{1,0:T(8,128)(2,1)} %patched.1.wait_ref.own_ref) | copy-start | bytes 1572868 | tf_op jit(solution)/shard_map/cond
  123.0 4.9 %collective-permute-start.6 = (f32[1,1024]{1,0:T(1,128)S(1)}, f32[1,1024]{1,0:T(1,128)S(1)}, u32[]{:S(2)}, u32[]{:S(2)}) collective-permute-start(f32[1,1024]{1,0:T(1,128)S(1)} %bitcast.42), channel_id=1, source_target_pairs={{0,1},{1,0},{2,3},{3,2},{4,5},{5,4},{6,7},{7,6},{8,9},{9,8},{10,11... | collective-permute-start | bytes 12296 | tf_op jit(solution)/shard_map/cond/branch_1_fun/ppermute | solution.py:33
  124.5 4.0 %collective-permute-start.7 = (f32[1,256]{1,0:T(1,128)S(1)}, f32[1,256]{1,0:T(1,128)S(1)}, u32[]{:S(2)}, u32[]{:S(2)}) collective-permute-start(f32[1,256]{1,0:T(1,128)S(1)} %bitcast.46), channel_id=1, source_target_pairs={{0,1},{1,0},{2,3},{3,2},{4,5},{5,4},{6,7},{7,6},{8,9},{9,8},{10,11... | collective-permute-start | bytes 3080 | tf_op jit(solution)/shard_map/cond/branch_1_fun/ppermute | solution.py:33
  127.7 6.0 %collective-permute-start.9 = (bf16[64,1024]{1,0:T(8,128)(2,1)}, bf16[64,1024]{1,0:T(8,128)(2,1)S(1)}, u32[]{:S(2)}, u32[]{:S(2)}) collective-permute-start(bf16[64,1024]{1,0:T(8,128)(2,1)} %get-tuple-element.94), channel_id=1, source_target_pairs={{0,4},{2,6},{4,0},{6,2},{8,12},{10,14},{12,8},{14,10},{16,20},{18,... | collective-permute-start | bytes 393224 | tf_op jit(solution)/shard_map/cond/branch_1_fun/ppermute | solution.py:33
  128.5 5.2 %copy-start.37 = (f32[1,256]{1,0:T(1,128)}, f32[1,256]{1,0:T(1,128)S(1)}, u32[]{:S(2)}) copy-start(f32[1,256]{1,0:T(1,128)S(1)} %collective-permute-done.7.refs_2_) | copy-start | bytes 3076 | tf_op jit(solution)/shard_map/cond
  133.7 0.8 copy-start.3
  134.5 3.0 %copy-start.38 = (f32[1,256]{1,0:T(1,128)S(1)}, f32[1,256]{1,0:T(1,128)}, u32[]{:S(2)}) copy-start(f32[1,256]{1,0:T(1,128)} %copy-done.37) | copy-start | bytes 3076 | tf_op jit(solution)/shard_map/cond
  136.6 2.9 %collective-permute-start.10 = (bf16[512,1024]{1,0:T(8,128)(2,1)}, bf16[512,1024]{1,0:T(8,128)(2,1)S(1)}, u32[]{:S(2)}, u32[]{:S(2)}) collective-permute-start(bf16[512,1024]{1,0:T(8,128)(2,1)} %pad_maximum_fusion), channel_id=1, source_target_pairs={{0,2},{2,0},{4,6},{6,4},{8,10},{10,8},{12,14},{14,12},{16,18},{18,... | collective-permute-start | bytes 3145736 | tf_op jit(solution)/shard_map/cond/branch_1_fun/ppermute | solution.py:33
  139.5 1.0 copy-start.16
  140.5 3.6 %copy-start.13 = (bf16[256,1024]{1,0:T(8,128)(2,1)S(1)}, bf16[256,1024]{1,0:T(8,128)(2,1)}, u32[]{:S(2)}) copy-start(bf16[256,1024]{1,0:T(8,128)(2,1)} %get-tuple-element.102.refs_0_) | copy-start | bytes 1572868 | tf_op jit(solution)/shard_map/cond
  144.1 2.8 %copy-start.40 = (bf16[80,1024]{1,0:T(8,128)(2,1)S(1)}, bf16[80,1024]{1,0:T(8,128)(2,1)}, u32[]{:S(2)}) copy-start(bf16[80,1024]{1,0:T(8,128)(2,1)} %get-tuple-element.98) | copy-start | bytes 491524 | tf_op jit(solution)/shard_map/cond
  144.1 5.6 %copy-start.39 = (bf16[80,1024]{1,0:T(8,128)(2,1)S(1)}, bf16[80,1024]{1,0:T(8,128)(2,1)}, u32[]{:S(2)}) copy-start(bf16[80,1024]{1,0:T(8,128)(2,1)} %get-tuple-element.99) | copy-start | bytes 491524 | tf_op jit(solution)/shard_map/cond
  144.1 6.0 %copy-start.1 = (bf16[1024,1024]{1,0:T(8,128)(2,1)S(1)}, bf16[1024,1024]{1,0:T(8,128)(2,1)}, u32[]{:S(2)}) copy-start(bf16[1024,1024]{1,0:T(8,128)(2,1)} %get-tuple-element.103) | copy-start | bytes 6291460 | tf_op jit(solution)/shard_map/cond
  144.1 19.4 %copy-start.6 = (f32[80,1024]{1,0:T(8,128)S(1)}, f32[80,1024]{1,0:T(8,128)}, u32[]{:S(2)}) copy-start(f32[80,1024]{1,0:T(8,128)} %get-tuple-element.96.refs_1_) | copy-start | bytes 983044 | tf_op jit(solution)/shard_map/cond
  144.1 14.4 %collective-permute-start.11 = (bf16[80,1024]{1,0:T(8,128)(2,1)}, bf16[80,1024]{1,0:T(8,128)(2,1)S(1)}, u32[]{:S(2)}, u32[]{:S(2)}) collective-permute-start(bf16[80,1024]{1,0:T(8,128)(2,1)} %get-tuple-element.97), channel_id=1, source_target_pairs={{0,8},{2,10},{4,12},{6,14},{8,0},{10,2},{12,4},{14,6},{16,24},{18,... | collective-permute-start | bytes 491528 | tf_op jit(solution)/shard_map/cond/branch_1_fun/ppermute | solution.py:33
  146.8 16.7 %collective-permute-start.12 = (bf16[80,1024]{1,0:T(8,128)(2,1)S(1)}, bf16[80,1024]{1,0:T(8,128)(2,1)S(1)}, u32[]{:S(2)}, u32[]{:S(2)}) collective-permute-start(bf16[80,1024]{1,0:T(8,128)(2,1)S(1)} %copy-done.40), channel_id=1, source_target_pairs={{0,16},{2,18},{4,20},{6,22},{8,24},{10,26},{12,28},{14,30},{16,0},... | collective-permute-start | bytes 491528 | tf_op jit(solution)/shard_map/cond/branch_1_fun/ppermute | solution.py:33
  149.7 13.9 %collective-permute-start.13 = (bf16[80,1024]{1,0:T(8,128)(2,1)S(1)}, bf16[80,1024]{1,0:T(8,128)(2,1)S(1)}, u32[]{:S(2)}, u32[]{:S(2)}) collective-permute-start(bf16[80,1024]{1,0:T(8,128)(2,1)S(1)} %copy-done.39), channel_id=1, source_target_pairs={{0,24},{2,26},{4,28},{6,30},{8,16},{10,18},{12,20},{14,22},{16,8},... | collective-permute-start | bytes 491528 | tf_op jit(solution)/shard_map/cond/branch_1_fun/ppermute | solution.py:33
  150.7 18.3 %copy-start.14 = (f32[256,512]{1,0:T(8,128)S(1)}, f32[256,512]{1,0:T(8,128)}, u32[]{:S(2)}) copy-start(f32[256,512]{1,0:T(8,128)} %after.8) | copy-start | bytes 1572868 | tf_op jit(solution)/shard_map/cond
  163.7 14.5 %collective-permute-start.16 = (bf16[80,1024]{1,0:T(8,128)(2,1)S(1)}, bf16[80,1024]{1,0:T(8,128)(2,1)S(1)}, u32[]{:S(2)}, u32[]{:S(2)}) collective-permute-start(bf16[80,1024]{1,0:T(8,128)(2,1)S(1)} %pad_maximum_fusion.4), channel_id=1, source_target_pairs={{0,8},{2,10},{4,12},{6,14},{8,0},{10,2},{12,4},{14,6},{16,24},{18,... | collective-permute-start | bytes 491528 | tf_op jit(solution)/shard_map/cond/branch_1_fun/ppermute | solution.py:33
  167.6 24.7 %copy-start.5 = (f32[256,1024]{1,0:T(8,128)S(1)}, f32[256,1024]{1,0:T(8,128)}, u32[]{:S(2)}) copy-start(f32[256,1024]{1,0:T(8,128)} %copy-done.4) | copy-start | bytes 3145732 | tf_op jit(solution)/shard_map/cond
  167.6 24.7 %copy-start.12 = (bf16[256,512]{1,0:T(8,128)(2,1)S(1)}, bf16[256,512]{1,0:T(8,128)(2,1)}, u32[]{:S(2)}) copy-start(bf16[256,512]{1,0:T(8,128)(2,1)} %get-tuple-element.100) | copy-start | bytes 786436 | tf_op jit(solution)/shard_map/cond
  167.6 24.7 %copy-start.18 = (bf16[256,512]{1,0:T(8,128)(2,1)S(1)}, bf16[256,512]{1,0:T(8,128)(2,1)}, u32[]{:S(2)}) copy-start(bf16[256,512]{1,0:T(8,128)(2,1)} %get-tuple-element.104) | copy-start | bytes 786436 | tf_op jit(solution)/shard_map/cond
  167.6 24.3 %collective-permute-start.17 = (f32[256,512]{1,0:T(8,128)S(1)}, f32[256,512]{1,0:T(8,128)S(1)}, u32[]{:S(2)}, u32[]{:S(2)}) collective-permute-start(f32[256,512]{1,0:T(8,128)S(1)} %slice_select_fusion.1), channel_id=1, source_target_pairs={{0,1},{1,0},{2,3},{3,2},{4,5},{5,4},{6,7},{7,6},{8,9},{9,8},{10,11... | collective-permute-start | bytes 1572872 | tf_op jit(solution)/shard_map/cond/branch_1_fun/ppermute | solution.py:33
  169.0 23.3 %collective-permute-start.18 = (f32[256,512]{1,0:T(8,128)S(1)}, f32[256,512]{1,0:T(8,128)S(1)}, u32[]{:S(2)}, u32[]{:S(2)}) collective-permute-start(f32[256,512]{1,0:T(8,128)S(1)} %copy-done.14), channel_id=1, source_target_pairs={{0,1},{1,0},{2,3},{3,2},{4,5},{5,4},{6,7},{7,6},{8,9},{9,8},{10,11... | collective-permute-start | bytes 1572872 | tf_op jit(solution)/shard_map/cond/branch_1_fun/ppermute | solution.py:33
  169.7 14.6 %collective-permute-start.15 = (bf16[80,1024]{1,0:T(8,128)(2,1)S(1)}, bf16[80,1024]{1,0:T(8,128)(2,1)S(1)}, u32[]{:S(2)}, u32[]{:S(2)}) collective-permute-start(bf16[80,1024]{1,0:T(8,128)(2,1)S(1)} %pad_maximum_fusion.4), channel_id=1, source_target_pairs={{0,16},{2,18},{4,20},{6,22},{8,24},{10,26},{12,28},{14,30},{16,0},... | collective-permute-start | bytes 491528 | tf_op jit(solution)/shard_map/cond/branch_1_fun/ppermute | solution.py:33
  170.4 21.2 %collective-permute-start.14 = (bf16[80,1024]{1,0:T(8,128)(2,1)S(1)}, bf16[80,1024]{1,0:T(8,128)(2,1)S(1)}, u32[]{:S(2)}, u32[]{:S(2)}) collective-permute-start(bf16[80,1024]{1,0:T(8,128)(2,1)S(1)} %pad_maximum_fusion.4), channel_id=1, source_target_pairs={{0,24},{2,26},{4,28},{6,30},{8,16},{10,18},{12,20},{14,22},{16,8},... | collective-permute-start | bytes 491528 | tf_op jit(solution)/shard_map/cond/branch_1_fun/ppermute | solution.py:33
  193.4 15.3 %collective-permute-start.28 = (bf16[320,1024]{1,0:T(8,128)(2,1)S(1)}, bf16[320,1024]{1,0:T(8,128)(2,1)S(1)}, u32[]{:S(2)}, u32[]{:S(2)}) collective-permute-start(bf16[320,1024]{1,0:T(8,128)(2,1)S(1)} %get-tuple-element.174.first_ref.rest_0_), channel_id=1, source_target_pairs={{0,4},{2,6},{4,0},{6,2},{8,12},{10,14},{12,8},{14,10},{16,20},{18,... | collective-permute-start | bytes 1966088 | tf_op jit(solution)/shard_map/ppermute | solution.py:33
  194.2 14.4 %collective-permute-start.30 = (bf16[320,1024]{1,0:T(8,128)(2,1)S(1)}, bf16[320,1024]{1,0:T(8,128)(2,1)S(1)}, u32[]{:S(2)}, u32[]{:S(2)}) collective-permute-start(bf16[320,1024]{1,0:T(8,128)(2,1)S(1)} %get-tuple-element.174.first_ref.rest_0_), channel_id=1, source_target_pairs={{0,2},{2,0},{4,6},{6,4},{8,10},{10,8},{12,14},{14,12},{16,18},{18,... | collective-permute-start | bytes 1966088 | tf_op jit(solution)/shard_map/ppermute | solution.py:33
  208.6 6.3 %copy-start.7 = (bf16[320,1024]{1,0:T(8,128)(2,1)}, bf16[320,1024]{1,0:T(8,128)(2,1)S(1)}, u32[]{:S(2)}) copy-start(bf16[320,1024]{1,0:T(8,128)(2,1)S(1)} %collective-permute-done.28.first_ref.rest_2_) | copy-start | bytes 1966084
  208.6 6.3 %collective-permute-start.29 = (bf16[320,1024]{1,0:T(8,128)(2,1)S(1)}, bf16[320,1024]{1,0:T(8,128)(2,1)S(1)}, u32[]{:S(2)}, u32[]{:S(2)}) collective-permute-start(bf16[320,1024]{1,0:T(8,128)(2,1)S(1)} %collective-permute-done.28.first_ref.rest_2_), channel_id=1, source_target_pairs={{0,2},{2,0},{4,6},{6,4},{8,10},{10,8},{12,14},{14,12},{16,18},{18,... | collective-permute-start | bytes 1966088 | tf_op jit(solution)/shard_map/ppermute | solution.py:33
  208.6 0.9 copy-start.9
  215.0 0.8 copy-start.8
  (9 other events, 6.0 us)
Sparse Core Ops, SparseCore 0:
  73.8 135.2 all-reduce.2

commit v20 on v19

--- a/solution.py
+++ b/solution.py
@@ -143,9 +143,12 @@
     conv_bias_ref,
     select_ref,
     mask_ref,
+    cot_ref,
+    other_cot_ref,
     convolved_ref,
     act_ref,
     selected_ref,
+    whole_cot_ref,
     inner,
 ):
     rows = act_ref.shape[0]
@@ -164,13 +167,17 @@
     @pl.when(pl.program_id(0) == 0)
     def _():
         selected_ref[...] = part
+        half = cot_ref.shape[1]
+        right = lax.axis_index("narrow") == 1
+        whole_cot_ref[:, :half] = jnp.where(right, other_cot_ref[...], cot_ref[...])
+        whole_cot_ref[:, half:] = jnp.where(right, cot_ref[...], other_cot_ref[...])
 
     @pl.when(pl.program_id(0) > 0)
     def _():
         selected_ref[...] += part
 
 
-def convolve(projected, conv_weight, conv_bias, select_weight, masks):
+def convolve(projected, conv_weight, conv_bias, select_weight, masks, cot, other_cot):
     parts, extended, width = projected.shape
     rows = extended - halo
     taps = conv_weight.shape[0]
@@ -185,12 +192,20 @@
             column_spec(1),
             column_spec(columns),
             whole_spec(rows, masks.shape[1]),
-        ],
-        [column_spec(rows), column_spec(rows), whole_spec(columns, rows)],
+            whole_spec(*cot.shape),
+            whole_spec(*cot.shape),
+        ],
+        [
+            column_spec(rows),
+            column_spec(rows),
+            whole_spec(columns, rows),
+            whole_spec(rows, 2 * cot.shape[1]),
+        ],
         [
             jax.ShapeDtypeStruct((rows, width), f32),
             jax.ShapeDtypeStruct((rows, width), bf16),
             jax.ShapeDtypeStruct((columns, rows), f32),
+            jax.ShapeDtypeStruct((rows, 2 * cot.shape[1]), bf16),
         ],
         [pltpu.VMEM((extended, scan_width), f32)],
         projected,
@@ -198,6 +213,8 @@
         conv_bias,
         select_weight,
         masks,
+        cot,
+        other_cot,
     )
 
 
@@ -1019,37 +1036,25 @@
         out_ref[n * rows : (n + 1) * rows, 0, :] = inner_ref[at : at + rows, :].astype(f32)
 
 
-def first_join_kernel(place_ref, gate_ref, first_ref, second_ref, low_ref, out_ref, wide_ref):
+def join_kernel(place_ref, gate_ref, low_ref, *rest, small_rows):
+    held = rest[:4]
+    out_ref, wide_ref, *row_refs, gain_ref, blocks = rest[4:]
     wide_ref[...] = low_ref[...].astype(f32)
-
-    @pl.when(pl.program_id(0) == 0)
-    def _():
-        put_quarter(out_ref, gate_ref, first_ref)
-
-    @pl.when(pl.program_id(0) == 1)
-    def _():
-        put_quarter(out_ref, gate_ref, second_ref)
-
-
-def last_join_kernel(place_ref, gate_ref, first_ref, second_ref, *rest, small_rows):
-    held = rest[:4]
-    out_ref, *row_refs, gain_ref, blocks = rest[5:]
-
-    @pl.when(pl.program_id(0) == 0)
-    def _():
-        put_quarter(out_ref, gate_ref, first_ref)
-
-    @pl.when(pl.program_id(0) == 1)
-    def _():
-        put_quarter(out_ref, gate_ref, second_ref)
-        rows = out_ref.shape[0] // 4
-        for flip, ref in enumerate(held):
+    rows = out_ref.shape[0] // 4
+    for flip, ref in enumerate(held):
+
+        @pl.when(pl.program_id(0) == flip)
+        def _():
+            put_quarter(out_ref, gate_ref, ref)
             number = place_ref[0] ^ flip
             number = (number & 1) * 2 + number // 2
             for n in range(4):
                 at = (number * 4 + n) * block_rows
                 taken = ref[(n + 1) * rows + n * block_rows : (n + 1) * (rows + block_rows), :]
                 blocks[pl.ds(pl.multiple_of(at, block_rows), block_rows), :] = taken.astype(f32)
+
+    @pl.when(pl.program_id(0) == 3)
+    def _():
         for ref, start in zip(row_refs, small_rows):
             for row in range(ref.shape[0]):
                 at = (start + row) // used_rows * block_rows + (start + row) % used_rows
@@ -1059,65 +1064,34 @@
         )
 
 
-def joined(kernel, place, flip, gate, first, second, specs, operands, out_specs, out_shape, scratch, aliases):
+def joined(place, gate, low, held, small_rows, small_counts):
     depth, width = gate.shape
     quarter = depth // 4
-
-    def target(j, place):
-        return place[0] ^ (flip + j)
-
-    whole = pl.BlockSpec(first.shape, lambda j, place: (0, 0))
+    whole = pl.BlockSpec(held[0].shape, lambda j, place: (0, 0))
+    part = pl.BlockSpec((quarter, width), lambda j, place: (j, 0))
     return pl.pallas_call(
-        kernel,
+        functools.partial(join_kernel, small_rows=small_rows),
         grid_spec=pltpu.PrefetchScalarGridSpec(
             num_scalar_prefetch=1,
-            grid=(2,),
-            in_specs=[
-                pl.BlockSpec((quarter, width), lambda j, place: (target(j, place), 0)),
-                whole,
-                whole,
+            grid=(4,),
+            in_specs=[pl.BlockSpec((quarter, width), lambda j, place: (place[0] ^ j, 0)), part]
+            + [whole] * 4,
+            out_specs=[
+                pl.BlockSpec((quarter, 2, width), lambda j, place: (place[0] ^ j, 0, 0)),
+                part,
             ]
-            + specs,
-            out_specs=[
-                pl.BlockSpec((quarter, 2, width), lambda j, place: (target(j, place), 0, 0))
-            ]
-            + out_specs,
-            scratch_shapes=scratch,
+            + [pl.BlockSpec((rows, width), lambda j, place: (0, 0)) for rows in small_counts],
+            scratch_shapes=[pltpu.VMEM((16 * block_rows, width), f32)],
         ),
-        out_shape=[jax.ShapeDtypeStruct((depth, 2, width), f32)] + out_shape,
-        input_output_aliases=aliases,
+        out_shape=[
+            jax.ShapeDtypeStruct((depth, 2, width), f32),
+            jax.ShapeDtypeStruct(low.shape, f32),
+        ]
+        + [jax.ShapeDtypeStruct((rows, width), f32) for rows in small_counts],
         compiler_params=pltpu.CompilerParams(vmem_limit_bytes=vmem_bytes),
         cost_estimate=tiny_cost,
         name="joined",
-    )(place, gate, first, second, *operands)
-
-
-def joined_first(place, gate, first, second, low):
-    rows, width = low.shape
-    half = pl.BlockSpec((rows // 2, width), lambda j, place: (j, 0))
-    kind = jax.ShapeDtypeStruct((rows, width), f32)
-    return joined(
-        first_join_kernel, place, 0, gate, first, second, [half], [low], [half], [kind], [], {}
-    )
-
-
-def joined_last(place, gate, held, begun, small_rows, small_counts):
-    width = gate.shape[1]
-    whole = pl.BlockSpec(held[0].shape, lambda j, place: (0, 0))
-    return joined(
-        functools.partial(last_join_kernel, small_rows=small_rows),
-        place,
-        2,
-        gate,
-        held[2],
-        held[3],
-        [whole] * 4 + [pl.BlockSpec(memory_space=pl.ANY)],
-        [*held, begun],
-        [pl.BlockSpec((rows, width), lambda j, place: (0, 0)) for rows in small_counts],
-        [jax.ShapeDtypeStruct((rows, width), f32) for rows in small_counts],
-        [pltpu.VMEM((16 * block_rows, width), f32)],
-        {8: 0},
-    )
+    )(place, gate, low, *held)
 
 
 def through(decay, total):
@@ -1197,11 +1171,6 @@
     count = decay_log.shape[0]
     right_half = lax.axis_index("narrow") == 1
 
-    def both_halves(own, other):
-        return jnp.concatenate(
-            [jnp.where(right_half, other, own), jnp.where(right_half, own, other)], axis=1
-        )
-
     other_tokens = swapped(tokens, "narrow", 1)
     other_cot = swapped(cotangent, "narrow", 1)
     edge, other_edge = to_next_both(edge_rows_of(segment_ids, tokens))
@@ -1212,11 +1181,10 @@
     projected = jnp.einsum(
         "td,dce->cte", normed_ext, in_weight, preferred_element_type=f32
     ).astype(bf16)
-    convolved, act, selected = convolve(
-        projected, conv_weight, conv_bias[None], select_weight, masks
+    convolved, act, selected, cot_whole = convolve(
+        projected, conv_weight, conv_bias[None], select_weight, masks, cotangent, other_cot
     )
     other_selected = swapped(selected, "narrow", 1)
-    cot_whole = both_halves(cotangent, other_cot)
     gated_grad = lax.dot_general(
         cot_whole, out_weight, contract_last, preferred_element_type=f32
     )
@@ -1296,14 +1264,15 @@
         normed_part = jnp.einsum(
             "cte,dce->td", jnp.stack([inner_grad, gate_grad]), in_weight, preferred_element_type=f32
         )
-        gain_part = jnp.sum(normed_part * whole * inverse, axis=0, keepdims=True)
+        inverse_then = after(inverse, send)
+        gain_part = jnp.sum(normed_part * whole * inverse_then, axis=0, keepdims=True)
         row_part = jnp.sum(normed_part * norm_gain * whole, axis=1)[None]
         first_bits, *more_bits = group_bits(2)
         gain_sum = gain_part + swapped(gain_part, "narrow", 1)
         for bit in (bit for bits in more_bits for bit in bits):
             gain_sum = gain_sum + swapped(gain_sum, "wide", bit)
         row_theirs = swapped(row_part, "narrow", 1)
-        near = after(near, gain_sum, row_theirs, smalls[1])
+        near = after(near, gain_part, smalls[1])
         far = swapped(jnp.concatenate([inner_grad, near]), "wide", 1)
         keep, *sends = inner_quarter(
             (wide_place >> 2 & 3)[None],
@@ -1348,12 +1317,12 @@
     )
 
     core = swapped(held, "wide", 1)
-    begun, out_weight_grad = joined_first(four_place, gate_sum, held, core, out_sum)
     near = swapped(held, "wide", 2)
     far = swapped(near, "wide", 1)
     conv_at = rank + count + 2
     (
         in_weight_grad,
+        out_weight_grad,
         step_weight_grad,
         decay_log_grad,
         skip_gain_grad,
@@ -1362,11 +1331,11 @@
         conv_weight_grad,
         conv_bias_grad,
         norm_gain_grad,
-    ) = joined_last(
+    ) = joined(
         four_place,
         gate_sum,
+        out_sum,
         (held, core, near, far),
-        begun,
         (0, rank, rank + count, rank + count + 1, conv_at, conv_at + columns, conv_at + columns + taps),
         (rank, count, 1, 1, columns, taps, 1, 1),
     )

time: 228 us -> 231 us (1.013)
  starting transfers between devices: 45.7 us -> 48.3 us
  matrix products: 9.88 us -> 12.2 us
    ppermute x26, starting transfers between devices: 32.6 us -> 35.4 us  [swapped(): return lax.ppermute(array, axis, [(i, i ^ bit) for i in range(peers)])]
    pallas_call x2 -> x1, Pallas kernels: 10.5 us -> 8.91 us  [joined(): pl.pallas_call(functools.partial(join_kernel, small_rows=small_rows), gri...]
  transfers between devices with their start and end apart: 32 -> 32, of which waited for: 15 -> 15; matrix products, arithmetic and copies ran while one was open for 8% -> 8% of each run, Pallas kernels for 26% -> 23%
where the time goes in v20:
time: 231 us; the launch traced here: 229 us
  Pallas kernels  77.7 us (34%)
  waiting for transfers between devices  63.6 us (28%)
  starting transfers between devices  48.3 us (21%)
  between operations  14.2 us (6%)
  matrix products  12.2 us (5%)
  local copies, waits for them, and re-layouts  7.02 us (3%)
  other arithmetic  5.6 us (2%)
    ppermute x26, waiting for transfers between devices, swapped(): return lax.ppermute(array, axis, [(i, i ^ bit) for i in range(peers)])  61.3 us
    pallas_call x5, Pallas kernels, call(): pl.pallas_call(kernel, grid=(width // scan_width,), in_specs=in_specs, ou...  52.5 us
    ppermute x26, starting transfers between devices, swapped(): return lax.ppermute(array, axis, [(i, i ^ bit) for i in range(peers)])  35.4 us
    ppermute x4, starting transfers between devices, passed_along(): return lax.ppermute(array, axis, pairs)  11.6 us
    pallas_call x1, Pallas kernels, joined(): pl.pallas_call(functools.partial(join_kernel, small_rows=small_rows), gri...  8.91 us
    dot_general x1, matrix products, after_forward(): jnp.einsum('cte,dce->td', jnp.stack([inner_grad, gate_grad]), in_weight,...  4.67 us
  transfers between devices with their start and end apart: 32, of which 15 were waited for; matrix products, arithmetic and copies ran while one was open for 8% of the time, Pallas kernels for 23%

profile of v20, /device:TPU:0, one launch (start us, length us, event | category | flops | bytes accessed | tf_op | source)
XLA Modules:
  0.0 229.0 jit_solution(4960755655870747295)
XLA Ops:
  7.2 3.0 %collective-permute-start.19 = (bf16[256,512]{1,0:T(8,128)(2,1)}, bf16[256,512]{1,0:T(8,128)(2,1)S(1)}, u32[]{:S(2)}, u32[]{:S(2)}) collective-permute-start(bf16[256,512]{1,0:T(8,128)(2,1)} %own_ref.1), channel_id=1, source_target_pairs={{0,1},{1,0},{2,3},{3,2},{4,5},{5,4},{6,7},{7,6},{8,9},{9,8},{10,11... | collective-permute-start | bytes 786440 | tf_op jit(solution)/shard_map/ppermute | solution.py:33
  10.3 1.4 edge_rows.1
  11.6 1.3 collective-permute-start.21
  13.0 4.0 %collective-permute-start.20 = (bf16[16,512]{1,0:T(8,128)(2,1)}, bf16[16,512]{1,0:T(8,128)(2,1)S(1)}, u32[]{:S(2)}, u32[]{:S(2)}) collective-permute-start(bf16[16,512]{1,0:T(8,128)(2,1)} %edge_rows.1), channel_id=1, source_target_pairs={{0,2},{2,4},{4,6},{6,8},{8,10},{10,12},{12,14},{14,16},{16,18},{18... | collective-permute-start | bytes 49160 | tf_op jit(solution)/shard_map/ppermute | solution.py:28
  17.0 1.6 collective-permute-start.22
  19.3 2.2 normalized.1
  21.6 4.1 %fusion.26.inner_ref.gate_ref = bf16[2,272,1024]{2,1,0:T(8,128)(2,1)S(1)} fusion(bf16[1024,2,1024]{2,1,0:T(2,128)(2,1)} %param.17, bf16[272,1024]{1,0:T(8,128)(2,1)} %get-tuple-element.154), kind=kOutput, calls=%fused_computation.48 | convolution fusion | flops 1141407744 | bytes 5865472 | tf_op jit(solution)/shard_map/td,dce->cte/dot_general | solution.py:1181
  25.7 0.7 copy-done.27
  26.4 3.6 %convolve.1 = (f32[256,1024]{1,0:T(8,128)}, bf16[256,1024]{1,0:T(8,128)(2,1)S(1)}, f32[96,256]{1,0:T(8,128)S(1)}, bf16[256,1024]{1,0:T(8,128)(2,1)}) custom-call(bf16[2,272,1024]{2,1,0:T(8,128)(2,1)S(1)} %fusion.26.inner_ref.gate_ref, f32[4,1024]{1,0:T(4,128)S(1)} %copy-done.30, f32[1,1024]{1,0:T(1,128)} %bitcast.40, bf16[96,1024]{1,0:T(8,128)(2,1)S(1)} %copy-done.18, ...), custom_call_target="tpu_custom_call" | custom-call | flops 1 | bytes 1 | tf_op jit(solution)/shard_map/convolve/pallas_call | solution.py:127
  30.0 1.4 collective-permute-start.23
  31.4 1.8 fusion.32.gated_grad_ref
  33.2 1.5 collective-permute-done.23.other_ref
  34.7 10.0 %scan_ends.1 = (f32[256,1024]{1,0:T(8,128)}, f32[256,1024]{1,0:T(8,128)}, bf16[48,1024]{1,0:T(8,128)(2,1)}) custom-call(f32[96,256]{1,0:T(8,128)S(1)} %get-tuple-element.156.selected_ref, f32[96,256]{1,0:T(8,128)S(1)} %collective-permute-done.23.other_ref, bf16[64,1024]{1,0:T(8,128)(2,1)S(1)} %copy-done.22, f32[1,1024]{1,0:T(1,128)} %bitcast.41, ...), custom_call_target="tpu_custom_call" | custom-call | flops 1 | bytes 1 | tf_op jit(solution)/shard_map/scan_ends/pallas_call | solution.py:127
  44.7 1.6 collective-permute-done.24.other_ref
  46.4 1.7 carry_round.2
  48.1 1.7 collective-permute-start.25
  49.8 3.5 %collective-permute-done.25.other_ref = bf16[48,1024]{1,0:T(8,128)(2,1)} collective-permute-done((bf16[48,1024]{1,0:T(8,128)(2,1)}, bf16[48,1024]{1,0:T(8,128)(2,1)}, u32[]{:S(2)}, u32[]{:S(2)}) %collective-permute-start.25) | collective-permute-done | bytes 98336 | tf_op jit(solution)/shard_map/ppermute | solution.py:33
  53.2 1.8 carry_round.3
  55.0 4.6 %collective-permute-start.26 = (bf16[16,1024]{1,0:T(8,128)(2,1)}, bf16[16,1024]{1,0:T(8,128)(2,1)S(1)}, u32[]{:S(2)}, u32[]{:S(2)}) collective-permute-start(bf16[16,1024]{1,0:T(8,128)(2,1)} %get-tuple-element.165), channel_id=1, source_target_pairs={{0,8},{2,10},{4,12},{6,14},{8,16},{10,18},{12,20},{14,22},{16,24},... | collective-permute-start | bytes 98312 | tf_op jit(solution)/shard_map/ppermute | solution.py:28
  59.6 1.5 collective-permute-start.27
  62.1 11.3 %scan_forward.1 = (bf16[256,1024]{1,0:T(8,128)(2,1)}, bf16[256,1024]{1,0:T(8,128)(2,1)}, bf16[1024,1024]{1,0:T(8,128)(2,1)}, bf16[1024,1024]{1,0:T(8,128)(2,1)}, f32[16,1024]{1,0:T(8,128)}) custom-call(f32[96,256]{1,0:T(8,128)} %copy-done.16, f32[96,256]{1,0:T(8,128)} %copy-done.17, f32[256,1024]{1,0:T(8,128)} %get-tuple-element.160.step_ref, ...), custom_call_target="tpu_custom_call" | custom-call | flops 1 | bytes 1 | tf_op jit(solution)/shard_map/scan_forward/pallas_call | solution.py:127
  73.5 124.9 %conditional.1 = (bf16[320,1024]{1,0:T(8,128)(2,1)}, bf16[256,512]{1,0:T(8,128)(2,1)}, bf16[256,512]{1,0:T(8,128)(2,1)}) conditional(s32[]{:T(128)} %convert_element_type.43, () %tuple.16, (s32[]{:T(128)}, f32[1024]{0:T(1024)}, f32[96,256]{1,0:T(8,128)}, f32[96,256]{1,0:T(8,128)}, f32[256,1024]{1,0:T(8,128)}, /*index=5*/f32[256,1024]{1,0:T(8,128)}, ...), branch_computations={%region_0.0_spmd, %region_1.4_spmd} | conditional | flops 1621776640 | bytes 92203912 | solution.py:1312
  73.5 23.6 %scan_backward.1 = (f32[256,1024]{1,0:T(8,128)}, f32[96,256]{1,0:T(8,128)}, f32[82,1024]{1,0:T(8,128)}) custom-call(f32[96,256]{1,0:T(8,128)} %get-tuple-element.64.selected_ref, f32[96,256]{1,0:T(8,128)} %get-tuple-element.65.other_ref, f32[256,1024]{1,0:T(8,128)} %get-tuple-element.66.step_pre_ref, f32[256,1024]{1,0:T(8,128)} %get-tuple-element.67.step_ref, ...), custom_call_target="tpu_custom_call" | custom-call | flops 1 | bytes 1 | tf_op jit(solution)/shard_map/cond/branch_1_fun/scan_backward/pallas_call | solution.py:127
  97.0 1.5 collective-permute-start
  98.6 0.8 constant_dynamic-slice_fusion
  99.4 0.7 collective-permute-start.3
  100.1 1.4 collective-permute-start.2
  102.0 4.1 %convolve_grad.1 = (bf16[256,1024]{1,0:T(8,128)(2,1)}, f32[8,1024]{1,0:T(8,128)}, f32[8,1024]{1,0:T(8,128)}, f32[101,1024]{1,0:T(8,128)}) custom-call(f32[96,256]{1,0:T(8,128)} %get-tuple-element.78.select_grad_ref.refs_1_, f32[96,256]{1,0:T(8,128)} %collective-permute-done.other_ref, bf16[96,1024]{1,0:T(8,128)(2,1)} %get-tuple-element.79.select_ref, ...), custom_call_target="tpu_custom_call" | custom-call | flops 1 | bytes 1 | tf_op jit(solution)/shard_map/cond/branch_1_fun/convolve_grad/pallas_call | solution.py:127
  106.1 1.5 collective-permute-start.1
  107.6 1.8 collective-permute-done.1.next_ref
  110.2 1.5 patched.1.wait_ref.own_ref
  111.7 2.3 small_halves.1
  114.0 1.6 collective-permute-start.6
  115.6 2.6 %collective-permute-start.5 = (bf16[256,1024]{1,0:T(8,128)(2,1)}, bf16[256,1024]{1,0:T(8,128)(2,1)S(1)}, u32[]{:S(2)}, u32[]{:S(2)}) collective-permute-start(bf16[256,1024]{1,0:T(8,128)(2,1)} %patched.1.wait_ref.own_ref), channel_id=1, source_target_pairs={{0,4},{2,6},{4,0},{6,2},{8,12},{10,14},{12,8},{14,10},{16,20},{18,... | collective-permute-start | bytes 1572872 | tf_op jit(solution)/shard_map/cond/branch_1_fun/ppermute | solution.py:33
  118.4 0.7 copy-done.29
  119.1 1.9 folded.1
  121.0 1.2 collective-permute-start.7
  122.3 4.7 %fusion.7 = (f32[256]{0:T(256)S(1)}, f32[1024]{0:T(1024)}, f32[256,1024]{1,0:T(8,128)S(1)}) fusion(bf16[256,1024]{1,0:T(8,128)(2,1)S(1)} %copy-done.38, f32[1024]{0:T(1024)S(1)} %copy-done.34, f32[256]{0:T(256)S(1)} %reduce, bf16[1024,2,1024]{2,1,0:T(2,128)(2,1)} %get-tuple-element.240, bf16[1,256,1024]{2,1,0:T(8,128)(2,1)S(1)} %bitcast.45, ...), kind=kOutput, calls=%fused_computation.7 | convolution fusion | flops 1076099840 | bytes 6825984 | tf_op jit(solution)/shard_map/cond/branch_1_fun/cte,dce->td/dot_general | solution.py:1264
  127.0 9.7 %collective-permute-done.7.refs_2_.arrived_ref = bf16[64,1024]{1,0:T(8,128)(2,1)S(1)} collective-permute-done((bf16[64,1024]{1,0:T(8,128)(2,1)}, bf16[64,1024]{1,0:T(8,128)(2,1)S(1)}, u32[]{:S(2)}, u32[]{:S(2)}) %collective-permute-start.7) | collective-permute-done | bytes 131104 | tf_op jit(solution)/shard_map/cond/branch_1_fun/ppermute | solution.py:33
  137.5 2.1 pad_maximum_fusion
  139.6 1.5 collective-permute-start.12
  141.7 0.9 slice_select_fusion.refs_0_
  142.6 2.1 collective-permute-done.18
  144.8 0.9 copy-done.12
  145.7 3.5 %inner_quarter.1 = (f32[80,1024]{1,0:T(8,128)}, bf16[80,1024]{1,0:T(8,128)(2,1)}, bf16[80,1024]{1,0:T(8,128)(2,1)}, bf16[80,1024]{1,0:T(8,128)(2,1)}) custom-call(s32[1]{0:T(128)} %bitcast.place_ref, bf16[256,1024]{1,0:T(8,128)(2,1)} %patched.1.wait_ref.own_ref, bf16[256,1024]{1,0:T(8,128)(2,1)} %after.8.near_ref, bf16[512,1024]{1,0:T(8,128)(2,1)} %copy-done.12, ...), custom_call_target="tpu_custom_call" | custom-call | flops 1 | bytes 1 | tf_op jit(solution)/shard_map/cond/branch_1_fun/inner_quarter/pallas_call | solution.py:1017
  149.3 1.6 collective-permute-start.9
  150.8 2.4 %collective-permute-start.10 = (bf16[80,1024]{1,0:T(8,128)(2,1)S(1)}, bf16[80,1024]{1,0:T(8,128)(2,1)S(1)}, u32[]{:S(2)}, u32[]{:S(2)}) collective-permute-start(bf16[80,1024]{1,0:T(8,128)(2,1)S(1)} %copy-done.41), channel_id=1, source_target_pairs={{0,16},{2,18},{4,20},{6,22},{8,24},{10,26},{12,28},{14,30},{16,0},... | collective-permute-start | bytes 491528 | tf_op jit(solution)/shard_map/cond/branch_1_fun/ppermute | solution.py:33
  153.2 0.8 collective-permute-start.11
  154.0 1.7 fusion.31
  155.8 2.8 %collective-permute-done.9 = bf16[80,1024]{1,0:T(8,128)(2,1)S(1)} collective-permute-done((bf16[80,1024]{1,0:T(8,128)(2,1)}, bf16[80,1024]{1,0:T(8,128)(2,1)S(1)}, u32[]{:S(2)}, u32[]{:S(2)}) %collective-permute-start.9) | collective-permute-done | bytes 163872 | tf_op jit(solution)/shard_map/cond/branch_1_fun/ppermute | solution.py:33
  158.5 8.8 %collective-permute-done.10 = bf16[80,1024]{1,0:T(8,128)(2,1)S(1)} collective-permute-done((bf16[80,1024]{1,0:T(8,128)(2,1)S(1)}, bf16[80,1024]{1,0:T(8,128)(2,1)S(1)}, u32[]{:S(2)}, u32[]{:S(2)}) %collective-permute-start.10) | collective-permute-done | bytes 163872 | tf_op jit(solution)/shard_map/cond/branch_1_fun/ppermute | solution.py:33
  167.5 6.2 %collective-permute-start.15 = (bf16[80,1024]{1,0:T(8,128)(2,1)S(1)}, bf16[80,1024]{1,0:T(8,128)(2,1)S(1)}, u32[]{:S(2)}, u32[]{:S(2)}) collective-permute-start(bf16[80,1024]{1,0:T(8,128)(2,1)S(1)} %pad_maximum_fusion.4), channel_id=1, source_target_pairs={{0,8},{2,10},{4,12},{6,14},{8,0},{10,2},{12,4},{14,6},{16,24},{18,... | collective-permute-start | bytes 491528 | tf_op jit(solution)/shard_map/cond/branch_1_fun/ppermute | solution.py:33
  174.4 1.5 collective-permute-start.17
  175.9 1.9 collective-permute-start.14
  177.8 1.4 collective-permute-start.13
  179.3 2.9 %collective-permute-done.15 = bf16[80,1024]{1,0:T(8,128)(2,1)S(1)} collective-permute-done((bf16[80,1024]{1,0:T(8,128)(2,1)S(1)}, bf16[80,1024]{1,0:T(8,128)(2,1)S(1)}, u32[]{:S(2)}, u32[]{:S(2)}) %collective-permute-start.15) | collective-permute-done | bytes 163872 | tf_op jit(solution)/shard_map/cond/branch_1_fun/ppermute | solution.py:33
  182.2 9.6 %collective-permute-done.14 = bf16[80,1024]{1,0:T(8,128)(2,1)S(1)} collective-permute-done((bf16[80,1024]{1,0:T(8,128)(2,1)S(1)}, bf16[80,1024]{1,0:T(8,128)(2,1)S(1)}, u32[]{:S(2)}, u32[]{:S(2)}) %collective-permute-start.14) | collective-permute-done | bytes 163872 | tf_op jit(solution)/shard_map/cond/branch_1_fun/ppermute | solution.py:33
  191.8 4.4 %collective-permute-done.13 = bf16[80,1024]{1,0:T(8,128)(2,1)S(1)} collective-permute-done((bf16[80,1024]{1,0:T(8,128)(2,1)S(1)}, bf16[80,1024]{1,0:T(8,128)(2,1)S(1)}, u32[]{:S(2)}, u32[]{:S(2)}) %collective-permute-start.13) | collective-permute-done | bytes 163872 | tf_op jit(solution)/shard_map/cond/branch_1_fun/ppermute | solution.py:33
  196.4 0.9 pad_maximum_fusion.1
  197.3 1.1 fusion.15
  198.4 11.9 %collective-permute-done.29.rest_2_ = bf16[320,1024]{1,0:T(8,128)(2,1)S(1)} collective-permute-done((bf16[320,1024]{1,0:T(8,128)(2,1)}, bf16[320,1024]{1,0:T(8,128)(2,1)S(1)}, u32[]{:S(2)}, u32[]{:S(2)}) %collective-permute-start.29) | collective-permute-done | bytes 655392 | tf_op jit(solution)/shard_map/ppermute | solution.py:33
  210.3 2.1 collective-permute-done.30.rest_3_
  212.4 0.8 copy-done.21
  213.2 8.9 %joined.1 = (f32[1024,2,1024]{2,1,0:T(2,128)}, f32[1024,1024]{1,0:T(8,128)}, f32[64,1024]{1,0:T(8,128)}, f32[16,1024]{1,0:T(8,128)}, f32[1,1024]{1,0:T(1,128)}, ...) custom-call(s32[1]{0:T(128)} %bitcast.19.place_ref, ...), custom_call_target="tpu_custom_call" | custom-call | flops 1 | bytes 1 | tf_op jit(solution)/shard_map/joined/pallas_call | solution.py:1072
  (127 shorter events, 6.0 us)
Async XLA Ops:
  7.2 205.2 %all-reduce.3.cloned.1.call-start = ((), (), s32[]{:S(2)}) async-start(), calls=%async_computation | async-start | bytes 8388608 | tf_op jit(solution)/shard_map/psum | solution.py:1219
  7.2 11.4 %collective-permute-start.19 = (bf16[256,512]{1,0:T(8,128)(2,1)}, bf16[256,512]{1,0:T(8,128)(2,1)S(1)}, u32[]{:S(2)}, u32[]{:S(2)}) collective-permute-start(bf16[256,512]{1,0:T(8,128)(2,1)} %own_ref.1), channel_id=1, source_target_pairs={{0,1},{1,0},{2,3},{3,2},{4,5},{5,4},{6,7},{7,6},{8,9},{9,8},{10,11... | collective-permute-start | bytes 786440 | tf_op jit(solution)/shard_map/ppermute | solution.py:33
  11.6 7.0 %collective-permute-start.21 = (bf16[16,512]{1,0:T(8,128)(2,1)}, bf16[16,512]{1,0:T(8,128)(2,1)S(1)}, u32[]{:S(2)}, u32[]{:S(2)}) collective-permute-start(bf16[16,512]{1,0:T(8,128)(2,1)} %edge_rows.1), channel_id=1, source_target_pairs={{0,3},{1,2},{2,5},{3,4},{4,7},{5,6},{6,9},{7,8},{8,11},{9,10},{10,... | collective-permute-start | bytes 49160 | tf_op jit(solution)/shard_map/ppermute | solution.py:51
  13.0 5.6 %collective-permute-start.20 = (bf16[16,512]{1,0:T(8,128)(2,1)}, bf16[16,512]{1,0:T(8,128)(2,1)S(1)}, u32[]{:S(2)}, u32[]{:S(2)}) collective-permute-start(bf16[16,512]{1,0:T(8,128)(2,1)} %edge_rows.1), channel_id=1, source_target_pairs={{0,2},{2,4},{4,6},{6,8},{8,10},{10,12},{12,14},{14,16},{16,18},{18... | collective-permute-start | bytes 49160 | tf_op jit(solution)/shard_map/ppermute | solution.py:28
  17.0 8.7 %collective-permute-start.22 = (bf16[256,512]{1,0:T(8,128)(2,1)}, bf16[256,512]{1,0:T(8,128)(2,1)S(1)}, u32[]{:S(2)}, u32[]{:S(2)}) collective-permute-start(bf16[256,512]{1,0:T(8,128)(2,1)} %cot_ref.1), channel_id=1, source_target_pairs={{0,1},{1,0},{2,3},{3,2},{4,5},{5,4},{6,7},{7,6},{8,9},{9,8},{10,11... | collective-permute-start | bytes 786440 | tf_op jit(solution)/shard_map/ppermute | solution.py:33
  21.6 4.8 %copy-start.13 = (bf16[256,512]{1,0:T(8,128)(2,1)S(1)}, bf16[256,512]{1,0:T(8,128)(2,1)}, u32[]{:S(2)}) copy-start(bf16[256,512]{1,0:T(8,128)(2,1)} %cot_ref.1) | copy-start | bytes 786436
  21.6 4.8 %copy-start.18 = (bf16[96,1024]{1,0:T(8,128)(2,1)S(1)}, bf16[96,1024]{1,0:T(8,128)(2,1)}, u32[]{:S(2)}) copy-start(bf16[96,1024]{1,0:T(8,128)(2,1)} %select_ref.1) | copy-start | bytes 589828
  21.6 4.8 %copy-start.30 = (f32[4,1024]{1,0:T(4,128)S(1)}, f32[4,1024]{1,0:T(4,128)}, u32[]{:S(2)}) copy-start(f32[4,1024]{1,0:T(4,128)} %conv_weight_ref.1) | copy-start | bytes 49156
  21.6 9.8 %copy-start = (bf16[1024,1024]{1,0:T(8,128)(2,1)S(1)}, bf16[1024,1024]{1,0:T(8,128)(2,1)}, u32[]{:S(2)}) copy-start(bf16[1024,1024]{1,0:T(8,128)(2,1)} %param.25) | copy-start | bytes 6291460
  30.0 14.7 %copy-start.16 = (f32[96,256]{1,0:T(8,128)}, f32[96,256]{1,0:T(8,128)S(1)}, u32[]{:S(2)}) copy-start(f32[96,256]{1,0:T(8,128)S(1)} %get-tuple-element.156.selected_ref) | copy-start | bytes 294916
  30.0 4.7 %copy-start.11 = (f32[16,1024]{1,0:T(8,128)S(1)}, f32[16,1024]{1,0:T(8,128)}, u32[]{:S(2)}) copy-start(f32[16,1024]{1,0:T(8,128)} %decay_log_ref.7) | copy-start | bytes 196612
  30.0 4.7 %copy-start.22 = (bf16[64,1024]{1,0:T(8,128)(2,1)S(1)}, bf16[64,1024]{1,0:T(8,128)(2,1)}, u32[]{:S(2)}) copy-start(bf16[64,1024]{1,0:T(8,128)(2,1)} %step_weight_ref.1) | copy-start | bytes 393220
  30.0 4.7 %collective-permute-start.23 = (f32[96,256]{1,0:T(8,128)S(1)}, f32[96,256]{1,0:T(8,128)S(1)}, u32[]{:S(2)}, u32[]{:S(2)}) collective-permute-start(f32[96,256]{1,0:T(8,128)S(1)} %get-tuple-element.156.selected_ref), channel_id=1, source_target_pairs={{0,1},{1,0},{2,3},{3,2},{4,5},{5,4},{6,7},{7,6},{8,9},{9,8},{10,11... | collective-permute-start | bytes 294920 | tf_op jit(solution)/shard_map/ppermute | solution.py:33
  34.7 10.0 %copy-start.17 = (f32[96,256]{1,0:T(8,128)}, f32[96,256]{1,0:T(8,128)S(1)}, u32[]{:S(2)}) copy-start(f32[96,256]{1,0:T(8,128)S(1)} %collective-permute-done.23.other_ref) | copy-start | bytes 294916
  44.6 1.7 collective-permute-start.24
  48.1 5.2 %collective-permute-start.25 = (bf16[48,1024]{1,0:T(8,128)(2,1)}, bf16[48,1024]{1,0:T(8,128)(2,1)}, u32[]{:S(2)}, u32[]{:S(2)}) collective-permute-start(bf16[48,1024]{1,0:T(8,128)(2,1)} %get-tuple-element.162.own_ref), channel_id=1, source_target_pairs={{0,4},{2,6},{4,0},{6,2},{8,12},{10,14},{12,8},{14,10},{16,20},{18,... | collective-permute-start | bytes 294920 | tf_op jit(solution)/shard_map/ppermute | solution.py:33
  55.0 6.5 %collective-permute-start.26 = (bf16[16,1024]{1,0:T(8,128)(2,1)}, bf16[16,1024]{1,0:T(8,128)(2,1)S(1)}, u32[]{:S(2)}, u32[]{:S(2)}) collective-permute-start(bf16[16,1024]{1,0:T(8,128)(2,1)} %get-tuple-element.165), channel_id=1, source_target_pairs={{0,8},{2,10},{4,12},{6,14},{8,16},{10,18},{12,20},{14,22},{16,24},... | collective-permute-start | bytes 98312 | tf_op jit(solution)/shard_map/ppermute | solution.py:28
  59.6 13.8 %collective-permute-start.27 = (bf16[16,1024]{1,0:T(8,128)(2,1)}, bf16[16,1024]{1,0:T(8,128)(2,1)}, u32[]{:S(2)}, u32[]{:S(2)}) collective-permute-start(bf16[16,1024]{1,0:T(8,128)(2,1)} %get-tuple-element.168), channel_id=1, source_target_pairs={{8,0},{10,2},{12,4},{14,6},{16,8},{18,10},{20,12},{22,14},{24,16},... | collective-permute-start | bytes 98312 | tf_op jit(solution)/shard_map/ppermute | solution.py:28
  97.0 5.0 %copy-start.15 = (f32[256,1024]{1,0:T(8,128)S(1)}, f32[256,1024]{1,0:T(8,128)}, u32[]{:S(2)}) copy-start(f32[256,1024]{1,0:T(8,128)} %get-tuple-element.81.convolved_ref) | copy-start | bytes 3145732 | tf_op jit(solution)/shard_map/cond
  97.0 5.0 %collective-permute-start = (f32[96,256]{1,0:T(8,128)}, f32[96,256]{1,0:T(8,128)}, u32[]{:S(2)}, u32[]{:S(2)}) collective-permute-start(f32[96,256]{1,0:T(8,128)} %get-tuple-element.78.select_grad_ref.refs_1_), channel_id=1, source_target_pairs={{0,1},{1,0},{2,3},{3,2},{4,5},{5,4},{6,7},{7,6},{8,9},{9,8},{10,11... | collective-permute-start | bytes 294920 | tf_op jit(solution)/shard_map/cond/branch_1_fun/ppermute | solution.py:33
  99.4 10.0 %collective-permute-start.4 = (bf16[256,256]{1,0:T(8,128)(2,1)}, bf16[256,256]{1,0:T(8,128)(2,1)S(1)}, u32[]{:S(2)}, u32[]{:S(2)}) collective-permute-start(bf16[256,256]{1,0:T(8,128)(2,1)} %get-tuple-element.257), channel_id=1, source_target_pairs={{0,6},{2,4},{4,2},{6,0},{8,14},{10,12},{12,10},{14,8},{16,22},{18,... | collective-permute-start | bytes 393224 | tf_op jit(solution)/shard_map/cond/branch_1_fun/ppermute | solution.py:33
  99.4 10.0 %collective-permute-start.3 = (bf16[256,256]{1,0:T(8,128)(2,1)}, bf16[256,256]{1,0:T(8,128)(2,1)S(1)}, u32[]{:S(2)}, u32[]{:S(2)}) collective-permute-start(bf16[256,256]{1,0:T(8,128)(2,1)} %get-tuple-element.258), channel_id=1, source_target_pairs={{0,2},{2,0},{4,6},{6,4},{8,10},{10,8},{12,14},{14,12},{16,18},{18,... | collective-permute-start | bytes 393224 | tf_op jit(solution)/shard_map/cond/branch_1_fun/ppermute | solution.py:33
  100.1 9.3 %collective-permute-start.2 = (bf16[256,256]{1,0:T(8,128)(2,1)}, bf16[256,256]{1,0:T(8,128)(2,1)S(1)}, u32[]{:S(2)}, u32[]{:S(2)}) collective-permute-start(bf16[256,256]{1,0:T(8,128)(2,1)} %get-tuple-element.259), channel_id=1, source_target_pairs={{0,4},{2,6},{4,0},{6,2},{8,12},{10,14},{12,8},{14,10},{16,20},{18,... | collective-permute-start | bytes 393224 | tf_op jit(solution)/shard_map/cond/branch_1_fun/ppermute | solution.py:33
  102.0 8.1 %copy-start.37 = (s32[256]{0:T(256)S(1)}, s32[256]{0:T(256)}, u32[]{:S(2)}) copy-start(s32[256]{0:T(256)} %get-tuple-element.63.ids_ref) | copy-start | bytes 3076 | tf_op jit(solution)/shard_map/cond
  106.1 3.3 %collective-permute-start.1 = (f32[8,1024]{1,0:T(8,128)}, f32[8,1024]{1,0:T(8,128)S(1)}, u32[]{:S(2)}, u32[]{:S(2)}) collective-permute-start(f32[8,1024]{1,0:T(8,128)} %get-tuple-element.85), channel_id=1, source_target_pairs={{2,0},{4,2},{6,4},{8,6},{10,8},{12,10},{14,12},{16,14},{18,16},{20... | collective-permute-start | bytes 98312 | tf_op jit(solution)/shard_map/cond/branch_1_fun/ppermute | solution.py:28
  109.4 0.7 copy-start.26
  110.2 12.1 %copy-start.34 = (f32[1024]{0:T(1024)S(1)}, f32[1024]{0:T(1024)}, u32[]{:S(2)}) copy-start(f32[1024]{0:T(1024)} %get-tuple-element.105) | copy-start | bytes 12292 | tf_op jit(solution)/shard_map/cond
  110.2 12.1 %copy-start.38 = (bf16[256,1024]{1,0:T(8,128)(2,1)S(1)}, bf16[256,1024]{1,0:T(8,128)(2,1)}, u32[]{:S(2)}) copy-start(bf16[256,1024]{1,0:T(8,128)(2,1)} %get-tuple-element.89) | copy-start | bytes 1572868 | tf_op jit(solution)/shard_map/cond
  110.2 12.1 %copy-start.39 = (bf16[256,1024]{1,0:T(8,128)(2,1)S(1)}, bf16[256,1024]{1,0:T(8,128)(2,1)}, u32[]{:S(2)}) copy-start(bf16[256,1024]{1,0:T(8,128)(2,1)} %get-tuple-element.87) | copy-start | bytes 1572868 | tf_op jit(solution)/shard_map/cond
  111.7 10.6 %copy-start.2 = (bf16[256,1024]{1,0:T(8,128)(2,1)S(1)}, bf16[256,1024]{1,0:T(8,128)(2,1)}, u32[]{:S(2)}) copy-start(bf16[256,1024]{1,0:T(8,128)(2,1)} %patched.1.wait_ref.own_ref) | copy-start | bytes 1572868 | tf_op jit(solution)/shard_map/cond
  114.0 4.4 %collective-permute-start.6 = (bf16[128,1024]{1,0:T(8,128)(2,1)}, bf16[128,1024]{1,0:T(8,128)(2,1)S(1)}, u32[]{:S(2)}, u32[]{:S(2)}) collective-permute-start(bf16[128,1024]{1,0:T(8,128)(2,1)} %get-tuple-element.94), channel_id=1, source_target_pairs={{0,2},{2,0},{4,6},{6,4},{8,10},{10,8},{12,14},{14,12},{16,18},{18,... | collective-permute-start | bytes 786440 | tf_op jit(solution)/shard_map/cond/branch_1_fun/ppermute | solution.py:33
  115.6 21.1 %collective-permute-start.5 = (bf16[256,1024]{1,0:T(8,128)(2,1)}, bf16[256,1024]{1,0:T(8,128)(2,1)S(1)}, u32[]{:S(2)}, u32[]{:S(2)}) collective-permute-start(bf16[256,1024]{1,0:T(8,128)(2,1)} %patched.1.wait_ref.own_ref), channel_id=1, source_target_pairs={{0,4},{2,6},{4,0},{6,2},{8,12},{10,14},{12,8},{14,10},{16,20},{18,... | collective-permute-start | bytes 1572872 | tf_op jit(solution)/shard_map/cond/branch_1_fun/ppermute | solution.py:33
  121.0 15.7 %collective-permute-start.7 = (bf16[64,1024]{1,0:T(8,128)(2,1)}, bf16[64,1024]{1,0:T(8,128)(2,1)S(1)}, u32[]{:S(2)}, u32[]{:S(2)}) collective-permute-start(bf16[64,1024]{1,0:T(8,128)(2,1)} %get-tuple-element.95.refs_1_), channel_id=1, source_target_pairs={{0,4},{2,6},{4,0},{6,2},{8,12},{10,14},{12,8},{14,10},{16,20},{18,... | collective-permute-start | bytes 393224 | tf_op jit(solution)/shard_map/cond/branch_1_fun/ppermute | solution.py:33
  127.0 17.8 %copy-start.4 = (f32[256,1024]{1,0:T(8,128)}, f32[256,1024]{1,0:T(8,128)S(1)}, u32[]{:S(2)}) copy-start(f32[256,1024]{1,0:T(8,128)S(1)} %get-tuple-element.267) | copy-start | bytes 3145732 | tf_op jit(solution)/shard_map/cond
  127.0 12.6 %copy-start.33 = (f32[1024]{0:T(1024)S(1)}, f32[1024]{0:T(1024)}, u32[]{:S(2)}) copy-start(f32[1024]{0:T(1024)} %get-tuple-element.250) | copy-start | bytes 12292 | tf_op jit(solution)/shard_map/cond
  136.7 0.9 copy-start.3
  139.6 5.2 %collective-permute-start.8 = (bf16[512,1024]{1,0:T(8,128)(2,1)}, bf16[512,1024]{1,0:T(8,128)(2,1)S(1)}, u32[]{:S(2)}, u32[]{:S(2)}) collective-permute-start(bf16[512,1024]{1,0:T(8,128)(2,1)} %pad_maximum_fusion), channel_id=1, source_target_pairs={{0,2},{2,0},{4,6},{6,4},{8,10},{10,8},{12,14},{14,12},{16,18},{18,... | collective-permute-start | bytes 3145736 | tf_op jit(solution)/shard_map/cond/branch_1_fun/ppermute | solution.py:33
  139.6 5.1 %collective-permute-start.12 = (f32[1,1024]{1,0:T(1,128)S(1)}, f32[1,1024]{1,0:T(1,128)S(1)}, u32[]{:S(2)}, u32[]{:S(2)}) collective-permute-start(f32[1,1024]{1,0:T(1,128)S(1)} %bitcast.36), channel_id=1, source_target_pairs={{0,1},{1,0},{2,3},{3,2},{4,5},{5,4},{6,7},{7,6},{8,9},{9,8},{10,11... | collective-permute-start | bytes 12296 | tf_op jit(solution)/shard_map/cond/branch_1_fun/ppermute | solution.py:33
  141.2 3.6 %collective-permute-start.18 = (f32[1,256]{1,0:T(1,128)S(1)}, f32[1,256]{1,0:T(1,128)S(1)}, u32[]{:S(2)}, u32[]{:S(2)}) collective-permute-start(f32[1,256]{1,0:T(1,128)S(1)} %bitcast.43), channel_id=1, source_target_pairs={{0,1},{1,0},{2,3},{3,2},{4,5},{5,4},{6,7},{7,6},{8,9},{9,8},{10,11... | collective-permute-start | bytes 3080 | tf_op jit(solution)/shard_map/cond/branch_1_fun/ppermute | solution.py:33
  144.8 1.0 copy-start.12
  145.7 3.5 %copy-start.8 = (bf16[256,1024]{1,0:T(8,128)(2,1)S(1)}, bf16[256,1024]{1,0:T(8,128)(2,1)}, u32[]{:S(2)}) copy-start(bf16[256,1024]{1,0:T(8,128)(2,1)} %get-tuple-element.103.refs_0_) | copy-start | bytes 1572868 | tf_op jit(solution)/shard_map/cond
  149.2 1.6 copy-start.41
  149.2 4.0 %copy-start.40 = (bf16[80,1024]{1,0:T(8,128)(2,1)S(1)}, bf16[80,1024]{1,0:T(8,128)(2,1)}, u32[]{:S(2)}) copy-start(bf16[80,1024]{1,0:T(8,128)(2,1)} %get-tuple-element.100) | copy-start | bytes 491524 | tf_op jit(solution)/shard_map/cond
  149.2 4.8 %copy-start.1 = (bf16[1024,1024]{1,0:T(8,128)(2,1)S(1)}, bf16[1024,1024]{1,0:T(8,128)(2,1)}, u32[]{:S(2)}) copy-start(bf16[1024,1024]{1,0:T(8,128)(2,1)} %get-tuple-element.104) | copy-start | bytes 6291460 | tf_op jit(solution)/shard_map/cond
  149.2 4.8 %copy-start.9 = (bf16[256,1024]{1,0:T(8,128)(2,1)}, bf16[256,1024]{1,0:T(8,128)(2,1)S(1)}, u32[]{:S(2)}) copy-start(bf16[256,1024]{1,0:T(8,128)(2,1)S(1)} %after.9) | copy-start | bytes 1572868 | tf_op jit(solution)/shard_map/cond
  149.3 18.1 %copy-start.6 = (f32[80,1024]{1,0:T(8,128)S(1)}, f32[80,1024]{1,0:T(8,128)}, u32[]{:S(2)}) copy-start(f32[80,1024]{1,0:T(8,128)} %get-tuple-element.97.refs_1_) | copy-start | bytes 983044 | tf_op jit(solution)/shard_map/cond
  149.3 9.3 %collective-permute-start.9 = (bf16[80,1024]{1,0:T(8,128)(2,1)}, bf16[80,1024]{1,0:T(8,128)(2,1)S(1)}, u32[]{:S(2)}, u32[]{:S(2)}) collective-permute-start(bf16[80,1024]{1,0:T(8,128)(2,1)} %get-tuple-element.98), channel_id=1, source_target_pairs={{0,8},{2,10},{4,12},{6,14},{8,0},{10,2},{12,4},{14,6},{16,24},{18,... | collective-permute-start | bytes 491528 | tf_op jit(solution)/shard_map/cond/branch_1_fun/ppermute | solution.py:33
  150.8 16.5 %collective-permute-start.10 = (bf16[80,1024]{1,0:T(8,128)(2,1)S(1)}, bf16[80,1024]{1,0:T(8,128)(2,1)S(1)}, u32[]{:S(2)}, u32[]{:S(2)}) collective-permute-start(bf16[80,1024]{1,0:T(8,128)(2,1)S(1)} %copy-done.41), channel_id=1, source_target_pairs={{0,16},{2,18},{4,20},{6,22},{8,24},{10,26},{12,28},{14,30},{16,0},... | collective-permute-start | bytes 491528 | tf_op jit(solution)/shard_map/cond/branch_1_fun/ppermute | solution.py:33
  153.2 14.1 %collective-permute-start.11 = (bf16[80,1024]{1,0:T(8,128)(2,1)S(1)}, bf16[80,1024]{1,0:T(8,128)(2,1)S(1)}, u32[]{:S(2)}, u32[]{:S(2)}) collective-permute-start(bf16[80,1024]{1,0:T(8,128)(2,1)S(1)} %copy-done.40), channel_id=1, source_target_pairs={{0,24},{2,26},{4,28},{6,30},{8,16},{10,18},{12,20},{14,22},{16,8},... | collective-permute-start | bytes 491528 | tf_op jit(solution)/shard_map/cond/branch_1_fun/ppermute | solution.py:33
  155.8 18.7 %copy-start.10 = (f32[256,512]{1,0:T(8,128)S(1)}, f32[256,512]{1,0:T(8,128)}, u32[]{:S(2)}) copy-start(f32[256,512]{1,0:T(8,128)} %after.10) | copy-start | bytes 1572868 | tf_op jit(solution)/shard_map/cond
  167.5 14.7 %collective-permute-start.15 = (bf16[80,1024]{1,0:T(8,128)(2,1)S(1)}, bf16[80,1024]{1,0:T(8,128)(2,1)S(1)}, u32[]{:S(2)}, u32[]{:S(2)}) collective-permute-start(bf16[80,1024]{1,0:T(8,128)(2,1)S(1)} %pad_maximum_fusion.4), channel_id=1, source_target_pairs={{0,8},{2,10},{4,12},{6,14},{8,0},{10,2},{12,4},{14,6},{16,24},{18,... | collective-permute-start | bytes 491528 | tf_op jit(solution)/shard_map/cond/branch_1_fun/ppermute | solution.py:33
  173.8 23.5 %copy-start.5 = (f32[256,1024]{1,0:T(8,128)S(1)}, f32[256,1024]{1,0:T(8,128)}, u32[]{:S(2)}) copy-start(f32[256,1024]{1,0:T(8,128)} %copy-done.4) | copy-start | bytes 3145732 | tf_op jit(solution)/shard_map/cond
  173.8 23.5 %copy-start.7 = (bf16[256,512]{1,0:T(8,128)(2,1)S(1)}, bf16[256,512]{1,0:T(8,128)(2,1)}, u32[]{:S(2)}) copy-start(bf16[256,512]{1,0:T(8,128)(2,1)} %get-tuple-element.101) | copy-start | bytes 786436 | tf_op jit(solution)/shard_map/cond
  173.8 23.5 %copy-start.14 = (bf16[256,512]{1,0:T(8,128)(2,1)S(1)}, bf16[256,512]{1,0:T(8,128)(2,1)}, u32[]{:S(2)}) copy-start(bf16[256,512]{1,0:T(8,128)(2,1)} %get-tuple-element.106) | copy-start | bytes 786436 | tf_op jit(solution)/shard_map/cond
  173.8 23.5 %collective-permute-start.16 = (f32[256,512]{1,0:T(8,128)S(1)}, f32[256,512]{1,0:T(8,128)S(1)}, u32[]{:S(2)}, u32[]{:S(2)}) collective-permute-start(f32[256,512]{1,0:T(8,128)S(1)} %slice_select_fusion.1), channel_id=1, source_target_pairs={{0,1},{1,0},{2,3},{3,2},{4,5},{5,4},{6,7},{7,6},{8,9},{9,8},{10,11... | collective-permute-start | bytes 1572872 | tf_op jit(solution)/shard_map/cond/branch_1_fun/ppermute | solution.py:33
  174.4 22.8 %collective-permute-start.17 = (f32[256,512]{1,0:T(8,128)S(1)}, f32[256,512]{1,0:T(8,128)S(1)}, u32[]{:S(2)}, u32[]{:S(2)}) collective-permute-start(f32[256,512]{1,0:T(8,128)S(1)} %copy-done.10), channel_id=1, source_target_pairs={{0,1},{1,0},{2,3},{3,2},{4,5},{5,4},{6,7},{7,6},{8,9},{9,8},{10,11... | collective-permute-start | bytes 1572872 | tf_op jit(solution)/shard_map/cond/branch_1_fun/ppermute | solution.py:33
  175.9 15.9 %collective-permute-start.14 = (bf16[80,1024]{1,0:T(8,128)(2,1)S(1)}, bf16[80,1024]{1,0:T(8,128)(2,1)S(1)}, u32[]{:S(2)}, u32[]{:S(2)}) collective-permute-start(bf16[80,1024]{1,0:T(8,128)(2,1)S(1)} %pad_maximum_fusion.4), channel_id=1, source_target_pairs={{0,16},{2,18},{4,20},{6,22},{8,24},{10,26},{12,28},{14,30},{16,0},... | collective-permute-start | bytes 491528 | tf_op jit(solution)/shard_map/cond/branch_1_fun/ppermute | solution.py:33
  177.8 18.4 %collective-permute-start.13 = (bf16[80,1024]{1,0:T(8,128)(2,1)S(1)}, bf16[80,1024]{1,0:T(8,128)(2,1)S(1)}, u32[]{:S(2)}, u32[]{:S(2)}) collective-permute-start(bf16[80,1024]{1,0:T(8,128)(2,1)S(1)} %pad_maximum_fusion.4), channel_id=1, source_target_pairs={{0,24},{2,26},{4,28},{6,30},{8,16},{10,18},{12,20},{14,22},{16,8},... | collective-permute-start | bytes 491528 | tf_op jit(solution)/shard_map/cond/branch_1_fun/ppermute | solution.py:33
  198.4 11.9 %collective-permute-start.29 = (bf16[320,1024]{1,0:T(8,128)(2,1)}, bf16[320,1024]{1,0:T(8,128)(2,1)S(1)}, u32[]{:S(2)}, u32[]{:S(2)}) collective-permute-start(bf16[320,1024]{1,0:T(8,128)(2,1)} %get-tuple-element.178.rest_0_), channel_id=1, source_target_pairs={{0,4},{2,6},{4,0},{6,2},{8,12},{10,14},{12,8},{14,10},{16,20},{18,... | collective-permute-start | bytes 1966088 | tf_op jit(solution)/shard_map/ppermute | solution.py:33
  198.4 11.9 %collective-permute-start.28 = (bf16[320,1024]{1,0:T(8,128)(2,1)}, bf16[320,1024]{1,0:T(8,128)(2,1)S(1)}, u32[]{:S(2)}, u32[]{:S(2)}) collective-permute-start(bf16[320,1024]{1,0:T(8,128)(2,1)} %get-tuple-element.178.rest_0_), channel_id=1, source_target_pairs={{0,2},{2,0},{4,6},{6,4},{8,10},{10,8},{12,14},{14,12},{16,18},{18,... | collective-permute-start | bytes 1966088 | tf_op jit(solution)/shard_map/ppermute | solution.py:33
  210.3 2.1 copy-start.19
  210.3 2.1 collective-permute-start.30
  210.3 2.1 copy-start.20
  212.4 0.8 copy-start.21
  (10 other events, 6.6 us)
Sparse Core Ops, SparseCore 0:
  73.6 135.0 all-reduce.2

commit v21 on v20

--- a/solution.py
+++ b/solution.py
@@ -92,14 +92,13 @@
     return blocks[0]
 
 
-def quarter_of_four(array):
-    width = array.shape[1] // 4
-    here = lax.axis_index("wide") & 3
-
-    def quarter(n):
-        return lax.dynamic_slice_in_dim(array, (here ^ n) * width, width, 1)
-
-    return [quarter(0)] + [swapped(quarter(n), "wide", n) for n in (2, 1, 3)]
+def core_columns(rows):
+    width = rows.shape[1] // 2
+    upper = is_upper(1).astype(jnp.int32)
+    return (
+        lax.dynamic_slice_in_dim(rows, upper * width, width, 1),
+        lax.dynamic_slice_in_dim(rows, (1 - upper) * width, width, 1),
+    )
 
 
 def silu_slope(values):
@@ -143,12 +142,9 @@
     conv_bias_ref,
     select_ref,
     mask_ref,
-    cot_ref,
-    other_cot_ref,
     convolved_ref,
     act_ref,
     selected_ref,
-    whole_cot_ref,
     inner,
 ):
     rows = act_ref.shape[0]
@@ -167,17 +163,13 @@
     @pl.when(pl.program_id(0) == 0)
     def _():
         selected_ref[...] = part
-        half = cot_ref.shape[1]
-        right = lax.axis_index("narrow") == 1
-        whole_cot_ref[:, :half] = jnp.where(right, other_cot_ref[...], cot_ref[...])
-        whole_cot_ref[:, half:] = jnp.where(right, cot_ref[...], other_cot_ref[...])
 
     @pl.when(pl.program_id(0) > 0)
     def _():
         selected_ref[...] += part
 
 
-def convolve(projected, conv_weight, conv_bias, select_weight, masks, cot, other_cot):
+def convolve(projected, conv_weight, conv_bias, select_weight, masks):
     parts, extended, width = projected.shape
     rows = extended - halo
     taps = conv_weight.shape[0]
@@ -192,20 +184,12 @@
             column_spec(1),
             column_spec(columns),
             whole_spec(rows, masks.shape[1]),
-            whole_spec(*cot.shape),
-            whole_spec(*cot.shape),
-        ],
-        [
-            column_spec(rows),
-            column_spec(rows),
-            whole_spec(columns, rows),
-            whole_spec(rows, 2 * cot.shape[1]),
-        ],
+        ],
+        [column_spec(rows), column_spec(rows), whole_spec(columns, rows)],
         [
             jax.ShapeDtypeStruct((rows, width), f32),
             jax.ShapeDtypeStruct((rows, width), bf16),
             jax.ShapeDtypeStruct((columns, rows), f32),
-            jax.ShapeDtypeStruct((rows, 2 * cot.shape[1]), bf16),
         ],
         [pltpu.VMEM((extended, scan_width), f32)],
         projected,
@@ -213,8 +197,6 @@
         conv_bias,
         select_weight,
         masks,
-        cot,
-        other_cot,
     )
 
 
@@ -745,7 +727,7 @@
     small_ref[columns + taps : columns + taps + 1, :] = jnp.sum(conv_grad, axis=0, keepdims=True)
     inner_grad_ref[...] = out.astype(bf16)
     before_ref[...] = before
-    last_ref[...] = out[rows - 8 :, :]
+    last_ref[...] = out[rows - halo :, :]
 
 
 def convolve_grad(
@@ -772,11 +754,11 @@
             whole_spec(rows, masks.shape[1]),
         ]
         + [pl.BlockSpec(memory_space=pl.ANY)] * len(waits),
-        [column_spec(rows), column_spec(8), column_spec(8), column_spec(small)],
+        [column_spec(rows), column_spec(8), column_spec(halo), column_spec(small)],
         [
             jax.ShapeDtypeStruct((rows, width), bf16),
             jax.ShapeDtypeStruct((8, width), f32),
-            jax.ShapeDtypeStruct((8, width), f32),
+            jax.ShapeDtypeStruct((halo, width), f32),
             jax.ShapeDtypeStruct((small, width), f32),
         ],
         [pltpu.VMEM((extended, scan_width), f32), pltpu.VMEM((rows + 16, scan_width), f32)],
@@ -803,6 +785,8 @@
     whole_ref,
     extended_ref,
     normed_ref,
+    chip_ref,
+    other_chip_ref,
     inverse_ref,
     mask_ref,
     rows_ref,
@@ -827,6 +811,10 @@
     normed = (whole * inverse * gain_ref[...]).astype(bf16)
     extended_ref[...] = normed
     normed_ref[...] = normed[:rows]
+    upper = lax.axis_index("wide") & 2 != 0
+    low, high = normed[:rows, :half], normed[:rows, half:]
+    chip_ref[...] = jnp.where(upper, high, low)
+    other_chip_ref[...] = jnp.where(upper, low, high)
     inverse_ref[...] = inverse[:rows]
 
 
@@ -839,6 +827,8 @@
             jax.ShapeDtypeStruct((rows, 2 * half), bf16),
             jax.ShapeDtypeStruct((extended, 2 * half), bf16),
             jax.ShapeDtypeStruct((rows, 2 * half), bf16),
+            jax.ShapeDtypeStruct((rows, half), bf16),
+            jax.ShapeDtypeStruct((rows, half), bf16),
             jax.ShapeDtypeStruct((rows, 1), f32),
             jax.ShapeDtypeStruct((rows, lanes), f32),
         ],
@@ -861,33 +851,31 @@
     )(array, *waits)
 
 
-def patch_kernel(ids_ref, rows_ref, last_ref, next_ref, *rest):
+def patch_kernel(ids_ref, last_ref, next_ref, wait_ref, out_ref):
     count = ids_ref.shape[0]
     place = lax.broadcasted_iota(jnp.int32, (8, 1), 0)
     same = jnp.zeros((8, 1), f32)
     for lag in range(8):
         here = jnp.where(ids_ref[count - 1 - lag] == ids_ref[count - 1], 1.0, 0.0)
         same = same + jnp.where(place == 7 - lag, here, 0.0)
-    total = last_ref[...] + next_ref[...] * same
-    rows = rows_ref[...].astype(f32)
-    rest[-1][...] = jnp.concatenate([rows[: halo - 8], total]).astype(bf16)
-
-
-def patched(ids, grads, last, following, *waits):
-    rows, width = grads.shape
-    block = pl.BlockSpec((halo, width), lambda j: (rows // halo - 1, 0))
-    edge = pl.BlockSpec((8, width), lambda j: (0, 0))
+    last = last_ref[...]
+    out_ref[...] = jnp.concatenate([last[:8], last[8:] + next_ref[...] * same]).astype(bf16)
+
+
+def patched(ids, last, following, wait):
+    vmem = pl.BlockSpec(memory_space=pltpu.VMEM)
     return pl.pallas_call(
         patch_kernel,
-        grid=(1,),
-        in_specs=[pl.BlockSpec(memory_space=pltpu.SMEM), block, edge, edge]
-        + [pl.BlockSpec(memory_space=pl.ANY)] * len(waits),
-        out_specs=block,
-        out_shape=jax.ShapeDtypeStruct((rows, width), bf16),
-        input_output_aliases={1: 0},
+        in_specs=[
+            pl.BlockSpec(memory_space=pltpu.SMEM),
+            vmem,
+            vmem,
+            pl.BlockSpec(memory_space=pl.ANY),
+        ],
+        out_shape=jax.ShapeDtypeStruct(last.shape, bf16),
         cost_estimate=tiny_cost,
         name="patched",
-    )(ids, grads, last, following, *waits)
+    )(ids, last, following, wait)
 
 
 def edge_kernel(ids_ref, tokens_ref, out_ref):
@@ -975,27 +963,15 @@
 
 
 def quarter_kernel(
-    place_ref,
-    own_ref,
-    near_ref,
-    far_ref,
-    normed_0,
-    normed_1,
-    normed_2,
-    normed_3,
-    small_ref,
-    arrived_ref,
-    *rest,
+    place_ref, ours_ref, far_ref, normed_ref, far_normed_ref, small_ref, arrived_ref, *rest
 ):
     keep_ref, *sends_refs, piece, small = rest[-6:]
-    total = None
-    tokens = own_ref.shape[0]
-    grads = (own_ref[...], near_ref[...], far_ref[:tokens, :], far_ref[tokens:, :])
-    for left, right in zip((normed_0, normed_1, normed_2, normed_3), grads):
-        part = lax.dot_general(left[...], right, contract_first, preferred_element_type=f32)
-        total = part if total is None else total + part
-    piece[...] = total
-    small[...] = small_ref[...] + arrived_ref[...].astype(f32)
+    piece[...] = lax.dot_general(
+        normed_ref[...], ours_ref[...], contract_first, preferred_element_type=f32
+    ) + lax.dot_general(
+        far_normed_ref[...], far_ref[...], contract_first, preferred_element_type=f32
+    )
+    small[...] = small_ref[...] + arrived_ref[: small.shape[0], :].astype(f32)
     rows, spare = piece.shape[0] // 4, small.shape[0] // 4
     for n in range(4):
         block = place_ref[0] ^ n
@@ -1009,23 +985,22 @@
             sends_refs[n - 1][rows:, :] = small_rows.astype(bf16)
 
 
-def inner_quarter(place, own, near, far, normed, smalls, waits):
-    width = own.shape[1]
-    quarter = normed[0].shape[1]
+def inner_quarter(place, ours, far, normed, far_normed, smalls):
+    width = ours.shape[1]
+    quarter = normed.shape[1]
     spare = smalls[0].shape[0]
     rows = (quarter + spare) // 4
     return pl.pallas_call(
         quarter_kernel,
         in_specs=[pl.BlockSpec(memory_space=pltpu.SMEM)]
-        + [pl.BlockSpec(memory_space=pltpu.VMEM)] * 9
-        + [pl.BlockSpec(memory_space=pl.ANY)] * len(waits),
+        + [pl.BlockSpec(memory_space=pltpu.VMEM)] * 6,
         out_shape=[jax.ShapeDtypeStruct((rows, width), f32)]
         + [jax.ShapeDtypeStruct((rows, width), bf16)] * 3,
         scratch_shapes=[pltpu.VMEM((quarter, width), f32), pltpu.VMEM((spare, width), f32)],
         compiler_params=pltpu.CompilerParams(vmem_limit_bytes=vmem_bytes),
         cost_estimate=tiny_cost,
         name="inner_quarter",
-    )(place, own, near, far, *normed, *smalls, *waits)
+    )(place, ours, far, normed, far_normed, *smalls)
 
 
 def put_quarter(out_ref, gate_ref, inner_ref):
@@ -1171,20 +1146,26 @@
     count = decay_log.shape[0]
     right_half = lax.axis_index("narrow") == 1
 
+    def both_halves(own, other):
+        return jnp.concatenate(
+            [jnp.where(right_half, other, own), jnp.where(right_half, own, other)], axis=1
+        )
+
     other_tokens = swapped(tokens, "narrow", 1)
     other_cot = swapped(cotangent, "narrow", 1)
     edge, other_edge = to_next_both(edge_rows_of(segment_ids, tokens))
 
-    whole_low, normed_ext, normed, inverse, masks = normalized(
+    whole_low, normed_ext, normed, normed_chip, normed_other_chip, inverse, masks = normalized(
         tokens, other_tokens, edge, other_edge, norm_gain[None], segment_ids[None]
     )
     projected = jnp.einsum(
         "td,dce->cte", normed_ext, in_weight, preferred_element_type=f32
     ).astype(bf16)
-    convolved, act, selected, cot_whole = convolve(
-        projected, conv_weight, conv_bias[None], select_weight, masks, cotangent, other_cot
+    convolved, act, selected = convolve(
+        projected, conv_weight, conv_bias[None], select_weight, masks
     )
     other_selected = swapped(selected, "narrow", 1)
+    cot_whole = both_halves(cotangent, other_cot)
     gated_grad = lax.dot_general(
         cot_whole, out_weight, contract_last, preferred_element_type=f32
     )
@@ -1242,7 +1223,7 @@
             skip_gain[None],
             step_weight,
         )
-        normed_four = quarter_of_four(after(normed, select_grad))
+        normed_near = swapped(normed_other_chip, "wide", 2)
         inner_main, before, last, conv_small = convolve_grad(
             select_grad,
             swapped(select_grad, "narrow", 1),
@@ -1255,33 +1236,36 @@
             masks,
             [],
         )
+        near = swapped(inner_main, "wide", 2)
         following = passed_along(before, "wide", -1)
-        inner_grad = patched(segment_ids, inner_main, last, following, *normed_four)
-        near = swapped(inner_grad, "wide", 2)
-        keep, send = small_halves(wide_place[None] & 1, scan_small, conv_small, inner_grad)
+        last_rows = patched(segment_ids, last, following, normed_near)
+        inner_grad = jnp.concatenate([inner_main[: rows - halo], last_rows])
+        normed_own, normed_send = core_columns(jnp.concatenate([normed_chip, normed_near]))
+        normed_far = swapped(normed_send, "wide", 1)
+        keep, send = small_halves(wide_place[None] & 1, scan_small, conv_small, last_rows)
         keep, send = folded((wide_place >> 1 & 1)[None], keep, swapped(send, "wide", 1))
-        smalls = [keep, swapped(send, "wide", 2)]
+        arrived = swapped(jnp.concatenate([send, last_rows]), "wide", 2)
         normed_part = jnp.einsum(
             "cte,dce->td", jnp.stack([inner_grad, gate_grad]), in_weight, preferred_element_type=f32
         )
-        inverse_then = after(inverse, send)
-        gain_part = jnp.sum(normed_part * whole * inverse_then, axis=0, keepdims=True)
+        gain_part = jnp.sum(normed_part * whole * inverse, axis=0, keepdims=True)
         row_part = jnp.sum(normed_part * norm_gain * whole, axis=1)[None]
         first_bits, *more_bits = group_bits(2)
-        gain_sum = gain_part + swapped(gain_part, "narrow", 1)
+        narrow_sums = jnp.concatenate([gain_part, row_part], axis=1)
+        narrow_sums = narrow_sums + swapped(narrow_sums, "narrow", 1)
+        gain_sum = narrow_sums[:, : 2 * features]
         for bit in (bit for bits in more_bits for bit in bits):
             gain_sum = gain_sum + swapped(gain_sum, "wide", bit)
-        row_theirs = swapped(row_part, "narrow", 1)
-        near = after(near, gain_part, smalls[1])
-        far = swapped(jnp.concatenate([inner_grad, near]), "wide", 1)
+        arrived = after(arrived, narrow_sums, normed_far)
+        ours = jnp.concatenate([inner_grad, near[: rows - halo], arrived[-halo:]])
+        far = swapped(ours, "wide", 1)
         keep, *sends = inner_quarter(
             (wide_place >> 2 & 3)[None],
-            inner_grad,
-            near,
+            ours,
             far,
-            normed_four,
-            smalls,
-            [],
+            normed_own,
+            normed_far,
+            (keep, arrived),
         )
         normed_mine, normed_other = narrow_halves(normed_part)
         normed_theirs = swapped(after(normed_other, keep), "narrow", 1)
@@ -1289,7 +1273,7 @@
         out_mine, out_other = narrow_halves(out_part)
         out_theirs = swapped(out_other, "narrow", 1)
         layer_out = (tokens.astype(f32) + (out_mine + out_theirs)).astype(bf16)
-        row_sum = (row_part + row_theirs).reshape(rows, 1)
+        row_sum = narrow_sums[:, 2 * features :].reshape(rows, 1)
         gain_mine = jnp.where(right_half, norm_gain[features:], norm_gain[:features])
         whole_grad = inverse * (gain_mine * (normed_mine + normed_theirs)) - tokens.astype(f32) * (
             inverse * inverse * inverse

time: 231 us -> 241 us (1.043)
  the two profiles are of different devices: /device:TPU:0 before, /device:TPU:21 now
where the time goes in v21:
time: 241 us; the launch traced here: 240 us
  waiting for transfers between devices  78.1 us (32%)
  Pallas kernels  77.6 us (32%)
  starting transfers between devices  40.4 us (17%)
  between operations  14.2 us (6%)
  local copies, waits for them, and re-layouts  12.1 us (5%)
  matrix products  10.8 us (4%)
  other arithmetic  6.66 us (3%)
    ppermute x24, waiting for transfers between devices, swapped(): return lax.ppermute(array, axis, [(i, i ^ bit) for i in range(peers)])  65.8 us
    pallas_call x5, Pallas kernels, call(): pl.pallas_call(kernel, grid=(width // scan_width,), in_specs=in_specs, ou...  52.2 us
    ppermute x24, starting transfers between devices, swapped(): return lax.ppermute(array, axis, [(i, i ^ bit) for i in range(peers)])  22.9 us
    ppermute x4, starting transfers between devices, passed_along(): return lax.ppermute(array, axis, pairs)  12.5 us
    ppermute x4, waiting for transfers between devices, passed_along(): return lax.ppermute(array, axis, pairs)  12.4 us
    pallas_call x1, Pallas kernels, joined(): pl.pallas_call(functools.partial(join_kernel, small_rows=small_rows), gri...  8.91 us
    ppermute x1, starting transfers between devices, to_next_both(): lax.ppermute(array, ('wide', 'narrow'), pairs)  4.9 us
  transfers between devices with their start and end apart: 30, of which 16 were waited for; matrix products, arithmetic and copies ran while one was open for 10% of the time, Pallas kernels for 23%

profile of v21, /device:TPU:21, one launch (start us, length us, event | category | flops | bytes accessed | tf_op | source)
XLA Modules:
  0.0 240.2 jit_solution(14877660535912667271)
XLA Ops:
  7.5 1.4 edge_rows.1
  8.9 4.9 %collective-permute-start.19 = (bf16[16,512]{1,0:T(8,128)(2,1)}, bf16[16,512]{1,0:T(8,128)(2,1)S(1)}, u32[]{:S(2)}, u32[]{:S(2)}) collective-permute-start(bf16[16,512]{1,0:T(8,128)(2,1)} %edge_rows.1), channel_id=1, source_target_pairs={{0,3},{1,2},{2,5},{3,4},{4,7},{5,6},{6,9},{7,8},{8,11},{9,10},{10,... | collective-permute-start | bytes 49160 | tf_op jit(solution)/shard_map/ppermute | solution.py:51
  13.8 1.9 collective-permute-start.18
  16.1 1.0 collective-permute-done.18.edge_ref
  17.8 2.7 %normalized.1 = (bf16[256,1024]{1,0:T(8,128)(2,1)}, bf16[272,1024]{1,0:T(8,128)(2,1)}, bf16[256,1024]{1,0:T(8,128)(2,1)}, bf16[256,512]{1,0:T(8,128)(2,1)}, bf16...) custom-call(bf16[256,512]{1,0:T(8,128)(2,1)} %own_ref.1, bf16[256,512]{1,0:T(8,128)(2,1)} %copy-done.19, ...), custom_call_target="tpu_custom_call" | custom-call | flops 1 | bytes 1 | tf_op jit(solution)/shard_map/normalized/pallas_call | solution.py:824
  20.5 4.0 %fusion.27.inner_ref.gate_ref = bf16[2,272,1024]{2,1,0:T(8,128)(2,1)S(1)} fusion(bf16[1024,2,1024]{2,1,0:T(2,128)(2,1)} %param.17, bf16[272,1024]{1,0:T(8,128)(2,1)} %get-tuple-element.156), kind=kOutput, calls=%fused_computation.52 | convolution fusion | flops 1141407744 | bytes 5865472 | tf_op jit(solution)/shard_map/td,dce->cte/dot_general | solution.py:1161
  24.5 3.1 %convolve.1 = (f32[256,1024]{1,0:T(8,128)}, bf16[256,1024]{1,0:T(8,128)(2,1)S(1)}, f32[96,256]{1,0:T(8,128)S(1)}) custom-call(bf16[2,272,1024]{2,1,0:T(8,128)(2,1)S(1)} %fusion.27.inner_ref.gate_ref, f32[4,1024]{1,0:T(4,128)S(1)} %copy-done.22, f32[1,1024]{1,0:T(1,128)} %bitcast.42, bf16[96,1024]{1,0:T(8,128)(2,1)S(1)} %copy-done.14, ...), custom_call_target="tpu_custom_call" | custom-call | flops 1 | bytes 1 | tf_op jit(solution)/shard_map/convolve/pallas_call | solution.py:126
  27.9 0.7 fusion.31.gated_grad_ref
  28.7 2.4 %collective-permute-done.20.other_ref = f32[96,256]{1,0:T(8,128)S(1)} collective-permute-done((f32[96,256]{1,0:T(8,128)S(1)}, f32[96,256]{1,0:T(8,128)S(1)}, u32[]{:S(2)}, u32[]{:S(2)}) %collective-permute-start.20) | collective-permute-done | bytes 98336 | tf_op jit(solution)/shard_map/ppermute | solution.py:33
  31.7 9.9 %scan_ends.1 = (f32[256,1024]{1,0:T(8,128)}, f32[256,1024]{1,0:T(8,128)}, bf16[48,1024]{1,0:T(8,128)(2,1)}) custom-call(f32[96,256]{1,0:T(8,128)S(1)} %get-tuple-element.158.selected_ref, f32[96,256]{1,0:T(8,128)S(1)} %collective-permute-done.20.other_ref, bf16[64,1024]{1,0:T(8,128)(2,1)S(1)} %copy-done.18, f32[1,1024]{1,0:T(1,128)} %bitcast.43, ...), custom_call_target="tpu_custom_call" | custom-call | flops 1 | bytes 1 | tf_op jit(solution)/shard_map/scan_ends/pallas_call | solution.py:126
  41.7 2.9 %collective-permute-start.22 = (bf16[48,1024]{1,0:T(8,128)(2,1)}, bf16[48,1024]{1,0:T(8,128)(2,1)}, u32[]{:S(2)}, u32[]{:S(2)}) collective-permute-start(bf16[48,1024]{1,0:T(8,128)(2,1)} %get-tuple-element.162.own_ref), channel_id=1, source_target_pairs={{0,2},{2,0},{4,6},{6,4},{8,10},{10,8},{12,14},{14,12},{16,18},{18,... | collective-permute-start | bytes 294920 | tf_op jit(solution)/shard_map/ppermute | solution.py:33
  44.6 1.3 collective-permute-done.22.other_ref
  45.9 1.7 carry_round.2
  47.9 4.0 %collective-permute-done.23.other_ref = bf16[48,1024]{1,0:T(8,128)(2,1)} collective-permute-done((bf16[48,1024]{1,0:T(8,128)(2,1)}, bf16[48,1024]{1,0:T(8,128)(2,1)}, u32[]{:S(2)}, u32[]{:S(2)}) %collective-permute-start.23) | collective-permute-done | bytes 98336 | tf_op jit(solution)/shard_map/ppermute | solution.py:33
  51.9 1.8 carry_round.3
  53.7 3.2 %collective-permute-start.24 = (bf16[16,1024]{1,0:T(8,128)(2,1)}, bf16[16,1024]{1,0:T(8,128)(2,1)S(1)}, u32[]{:S(2)}, u32[]{:S(2)}) collective-permute-start(bf16[16,1024]{1,0:T(8,128)(2,1)} %get-tuple-element.166), channel_id=1, source_target_pairs={{0,8},{2,10},{4,12},{6,14},{8,16},{10,18},{12,20},{14,22},{16,24},... | collective-permute-start | bytes 98312 | tf_op jit(solution)/shard_map/ppermute | solution.py:28
  56.9 2.3 collective-permute-start.25
  59.2 0.9 pad_maximum_fusion.7.cot_ref
  60.7 11.4 %scan_forward.1 = (bf16[256,1024]{1,0:T(8,128)(2,1)}, bf16[256,1024]{1,0:T(8,128)(2,1)}, bf16[1024,1024]{1,0:T(8,128)(2,1)}, bf16[1024,1024]{1,0:T(8,128)(2,1)}, f32[16,1024]{1,0:T(8,128)}) custom-call(f32[96,256]{1,0:T(8,128)S(1)} %get-tuple-element.158.selected_ref, f32[96,256]{1,0:T(8,128)} %copy-done.11, f32[256,1024]{1,0:T(8,128)} %get-tuple-element.161.step_ref, ...), custom_call_target="tpu_custom_call" | custom-call | flops 1 | bytes 1 | tf_op jit(solution)/shard_map/scan_forward/pallas_call | solution.py:126
  72.2 0.9 copy-done.4
  73.1 131.4 %conditional.1 = (bf16[320,1024]{1,0:T(8,128)(2,1)}, bf16[256,512]{1,0:T(8,128)(2,1)}, bf16[256,512]{1,0:T(8,128)(2,1)}) conditional(s32[]{:T(128)} %convert_element_type.44, () %tuple.16, (s32[]{:T(128)}, f32[1024]{0:T(1024)}, f32[96,256]{1,0:T(8,128)S(1)}, f32[96,256]{1,0:T(8,128)}, f32[256,1024]{1,0:T(8,128)}, /*index=5*/f32[256,1024]{1,0:T(8,128)}, ...), branch_computations={%region_0.1_spmd, %region_1.4_spmd} | conditional | flops 1625251584 | bytes 70999440 | solution.py:1296
  73.4 23.5 %scan_backward.1 = (f32[256,1024]{1,0:T(8,128)}, f32[96,256]{1,0:T(8,128)}, f32[82,1024]{1,0:T(8,128)}) custom-call(f32[96,256]{1,0:T(8,128)S(1)} %get-tuple-element.63.selected_ref, f32[96,256]{1,0:T(8,128)} %get-tuple-element.64.other_ref, f32[256,1024]{1,0:T(8,128)} %get-tuple-element.65.step_pre_ref, f32[256,1024]{1,0:T(8,128)} %get-tuple-element.66.step_ref, ...), custom_call_target="tpu_custom_call" | custom-call | flops 1 | bytes 1 | tf_op jit(solution)/shard_map/cond/branch_1_fun/scan_backward/pallas_call | solution.py:126
  97.3 1.0 copy.31
  98.2 1.0 constant_dynamic-update-slice_fusion.1
  99.2 1.8 collective-permute-done.other_ref
  101.7 4.2 %convolve_grad.1 = (bf16[256,1024]{1,0:T(8,128)(2,1)}, f32[8,1024]{1,0:T(8,128)}, f32[16,1024]{1,0:T(8,128)}, f32[101,1024]{1,0:T(8,128)}) custom-call(f32[96,256]{1,0:T(8,128)} %get-tuple-element.77.select_grad_ref, f32[96,256]{1,0:T(8,128)} %copy-done.21, bf16[96,1024]{1,0:T(8,128)(2,1)} %get-tuple-element.78.select_ref, ...), custom_call_target="tpu_custom_call" | custom-call | flops 1 | bytes 1 | tf_op jit(solution)/shard_map/cond/branch_1_fun/convolve_grad/pallas_call | solution.py:126
  105.9 1.1 slice.25
  107.0 1.2 collective-permute-start.3
  108.2 5.2 %collective-permute-start.1 = (f32[8,1024]{1,0:T(8,128)}, f32[8,1024]{1,0:T(8,128)S(1)}, u32[]{:S(2)}, u32[]{:S(2)}) collective-permute-start(f32[8,1024]{1,0:T(8,128)} %get-tuple-element.85), channel_id=1, source_target_pairs={{2,0},{4,2},{6,4},{8,6},{10,8},{12,10},{14,12},{16,14},{18,16},{20... | collective-permute-start | bytes 98312 | tf_op jit(solution)/shard_map/cond/branch_1_fun/ppermute | solution.py:28
  113.4 0.8 constant_dynamic-slice_fusion
  114.2 11.3 %collective-permute-done.1.next_ref = f32[8,1024]{1,0:T(8,128)S(1)} collective-permute-done((f32[8,1024]{1,0:T(8,128)}, f32[8,1024]{1,0:T(8,128)S(1)}, u32[]{:S(2)}, u32[]{:S(2)}) %collective-permute-start.1) | collective-permute-done | bytes 32800 | tf_op jit(solution)/shard_map/cond/branch_1_fun/ppermute | solution.py:28
  126.2 1.5 patched.1.wait_ref
  127.6 2.2 small_halves.1
  129.9 0.8 maximum_bitcast_fusion
  130.7 4.3 %fusion.6 = (f32[1024]{0:T(1024)S(1)}, f32[256]{0:T(256)S(1)}, f32[256,1024]{1,0:T(8,128)S(1)}) fusion(bf16[256,1024]{1,0:T(8,128)(2,1)} %get-tuple-element.94, f32[256]{0:T(256)S(1)} %bitcast.40, f32[1024]{0:T(1024)S(1)} %copy-done.26, bf16[1024,2,1024]{2,1,0:T(2,128)(2,1)} %get-tuple-element.213, bf16[1,256,1024]{2,1,0:T(8,128)(2,1)} %bitcast.48, ...), kind=kOutput, calls=%fused_computation.6 | convolution fusion | flops 1076099840 | bytes 6825984 | tf_op jit(solution)/shard_map/cond/branch_1_fun/cte,dce->td/dot_general | solution.py:1248
  135.4 0.7 copy-done.20
  136.1 1.9 folded.1
  138.0 0.9 pad_maximum_fusion.4
  139.6 1.1 slice.37
  140.7 6.3 %collective-permute-done.5.refs_0_ = bf16[80,1024]{1,0:T(8,128)(2,1)S(1)} collective-permute-done((bf16[80,1024]{1,0:T(8,128)(2,1)S(1)}, bf16[80,1024]{1,0:T(8,128)(2,1)S(1)}, u32[]{:S(2)}, u32[]{:S(2)}) %collective-permute-start.5) | collective-permute-done | bytes 163872 | tf_op jit(solution)/shard_map/cond/branch_1_fun/ppermute | solution.py:33
  147.7 0.8 slice.38
  148.5 0.9 collective-permute-start.8
  149.4 0.9 slice_select_fusion.refs_0_
  150.3 1.5 collective-permute-done.8.far_ref
  151.8 3.4 %inner_quarter.1 = (f32[80,1024]{1,0:T(8,128)}, bf16[80,1024]{1,0:T(8,128)(2,1)}, bf16[80,1024]{1,0:T(8,128)(2,1)}, bf16[80,1024]{1,0:T(8,128)(2,1)}) custom-call(s32[1]{0:T(128)} %bitcast.place_ref, bf16[512,1024]{1,0:T(8,128)(2,1)} %copy-done.2, bf16[512,1024]{1,0:T(8,128)(2,1)} %collective-permute-done.8.far_ref, ...), custom_call_target="tpu_custom_call" | custom-call | flops 1 | bytes 1 | tf_op jit(solution)/shard_map/cond/branch_1_fun/inner_quarter/pallas_call | solution.py:993
  155.3 1.3 collective-permute-start.9
  156.8 1.2 collective-permute-start.11
  158.0 1.8 fusion.32
  159.7 3.7 %collective-permute-done.9 = bf16[80,1024]{1,0:T(8,128)(2,1)S(1)} collective-permute-done((bf16[80,1024]{1,0:T(8,128)(2,1)}, bf16[80,1024]{1,0:T(8,128)(2,1)S(1)}, u32[]{:S(2)}, u32[]{:S(2)}) %collective-permute-start.9) | collective-permute-done | bytes 163872 | tf_op jit(solution)/shard_map/cond/branch_1_fun/ppermute | solution.py:33
  163.5 4.2 %collective-permute-done.10 = bf16[80,1024]{1,0:T(8,128)(2,1)S(1)} collective-permute-done((bf16[80,1024]{1,0:T(8,128)(2,1)}, bf16[80,1024]{1,0:T(8,128)(2,1)S(1)}, u32[]{:S(2)}, u32[]{:S(2)}) %collective-permute-start.10) | collective-permute-done | bytes 163872 | tf_op jit(solution)/shard_map/cond/branch_1_fun/ppermute | solution.py:33
  167.6 9.1 %collective-permute-done.11 = bf16[80,1024]{1,0:T(8,128)(2,1)S(1)} collective-permute-done((bf16[80,1024]{1,0:T(8,128)(2,1)}, bf16[80,1024]{1,0:T(8,128)(2,1)S(1)}, u32[]{:S(2)}, u32[]{:S(2)}) %collective-permute-start.11) | collective-permute-done | bytes 163872 | tf_op jit(solution)/shard_map/cond/branch_1_fun/ppermute | solution.py:33
  177.2 1.4 collective-permute-start.16
  178.6 2.6 %collective-permute-start.12 = (bf16[80,1024]{1,0:T(8,128)(2,1)S(1)}, bf16[80,1024]{1,0:T(8,128)(2,1)S(1)}, u32[]{:S(2)}, u32[]{:S(2)}) collective-permute-start(bf16[80,1024]{1,0:T(8,128)(2,1)S(1)} %pad_maximum_fusion.5), channel_id=1, source_target_pairs={{0,24},{2,26},{4,28},{6,30},{8,16},{10,18},{12,20},{14,22},{16,8},... | collective-permute-start | bytes 491528 | tf_op jit(solution)/shard_map/cond/branch_1_fun/ppermute | solution.py:33
  181.2 1.3 collective-permute-done.14
  182.6 4.7 %collective-permute-done.13 = bf16[80,1024]{1,0:T(8,128)(2,1)S(1)} collective-permute-done((bf16[80,1024]{1,0:T(8,128)(2,1)S(1)}, bf16[80,1024]{1,0:T(8,128)(2,1)S(1)}, u32[]{:S(2)}, u32[]{:S(2)}) %collective-permute-start.13) | collective-permute-done | bytes 163872 | tf_op jit(solution)/shard_map/cond/branch_1_fun/ppermute | solution.py:33
  187.3 15.0 %collective-permute-done.12 = bf16[80,1024]{1,0:T(8,128)(2,1)S(1)} collective-permute-done((bf16[80,1024]{1,0:T(8,128)(2,1)S(1)}, bf16[80,1024]{1,0:T(8,128)(2,1)S(1)}, u32[]{:S(2)}, u32[]{:S(2)}) %collective-permute-start.12) | collective-permute-done | bytes 163872 | tf_op jit(solution)/shard_map/cond/branch_1_fun/ppermute | solution.py:33
  202.5 0.9 pad_maximum_fusion.1
  203.4 1.1 fusion.15
  204.7 3.8 %collective-permute-start.26 = (bf16[320,1024]{1,0:T(8,128)(2,1)}, bf16[320,1024]{1,0:T(8,128)(2,1)S(1)}, u32[]{:S(2)}, u32[]{:S(2)}) collective-permute-start(bf16[320,1024]{1,0:T(8,128)(2,1)} %get-tuple-element.181.rest_0_), channel_id=1, source_target_pairs={{0,2},{2,0},{4,6},{6,4},{8,10},{10,8},{12,14},{14,12},{16,18},{18,... | collective-permute-start | bytes 1966088 | tf_op jit(solution)/shard_map/ppermute | solution.py:33
  208.5 8.7 %collective-permute-done.27.rest_2_ = bf16[320,1024]{1,0:T(8,128)(2,1)S(1)} collective-permute-done((bf16[320,1024]{1,0:T(8,128)(2,1)}, bf16[320,1024]{1,0:T(8,128)(2,1)S(1)}, u32[]{:S(2)}, u32[]{:S(2)}) %collective-permute-start.27) | collective-permute-done | bytes 655392 | tf_op jit(solution)/shard_map/ppermute | solution.py:33
  217.2 4.6 %collective-permute-start.28 = (bf16[320,1024]{1,0:T(8,128)(2,1)S(1)}, bf16[320,1024]{1,0:T(8,128)(2,1)S(1)}, u32[]{:S(2)}, u32[]{:S(2)}) collective-permute-start(bf16[320,1024]{1,0:T(8,128)(2,1)S(1)} %collective-permute-done.27.rest_2_), channel_id=1, source_target_pairs={{0,2},{2,0},{4,6},{6,4},{8,10},{10,8},{12,14},{14,12},{16,18},{18,... | collective-permute-start | bytes 1966088 | tf_op jit(solution)/shard_map/ppermute | solution.py:33
  221.9 1.7 collective-permute-done.28.rest_3_
  223.6 0.9 copy-done.17
  224.4 8.9 %joined.1 = (f32[1024,2,1024]{2,1,0:T(2,128)}, f32[1024,1024]{1,0:T(8,128)}, f32[64,1024]{1,0:T(8,128)}, f32[16,1024]{1,0:T(8,128)}, f32[1,1024]{1,0:T(1,128)}, ...) custom-call(s32[1]{0:T(128)} %bitcast.21.place_ref, ...), custom_call_target="tpu_custom_call" | custom-call | flops 1 | bytes 1 | tf_op jit(solution)/shard_map/joined/pallas_call | solution.py:1047
  (112 shorter events, 8.2 us)
Async XLA Ops:
  7.2 216.4 %all-reduce.3.cloned.1.call-start = ((), (), s32[]{:S(2)}) async-start(), calls=%async_computation | async-start | bytes 8388608 | tf_op jit(solution)/shard_map/psum | solution.py:1200
  7.2 9.9 %collective-permute-start.17 = (bf16[256,512]{1,0:T(8,128)(2,1)}, bf16[256,512]{1,0:T(8,128)(2,1)S(1)}, u32[]{:S(2)}, u32[]{:S(2)}) collective-permute-start(bf16[256,512]{1,0:T(8,128)(2,1)} %own_ref.1), channel_id=1, source_target_pairs={{0,1},{1,0},{2,3},{3,2},{4,5},{5,4},{6,7},{7,6},{8,9},{9,8},{10,11... | collective-permute-start | bytes 786440 | tf_op jit(solution)/shard_map/ppermute | solution.py:33
  8.9 7.2 %collective-permute-start.19 = (bf16[16,512]{1,0:T(8,128)(2,1)}, bf16[16,512]{1,0:T(8,128)(2,1)S(1)}, u32[]{:S(2)}, u32[]{:S(2)}) collective-permute-start(bf16[16,512]{1,0:T(8,128)(2,1)} %edge_rows.1), channel_id=1, source_target_pairs={{0,3},{1,2},{2,5},{3,4},{4,7},{5,6},{6,9},{7,8},{8,11},{9,10},{10,... | collective-permute-start | bytes 49160 | tf_op jit(solution)/shard_map/ppermute | solution.py:51
  13.8 3.3 %collective-permute-start.18 = (bf16[16,512]{1,0:T(8,128)(2,1)}, bf16[16,512]{1,0:T(8,128)(2,1)S(1)}, u32[]{:S(2)}, u32[]{:S(2)}) collective-permute-start(bf16[16,512]{1,0:T(8,128)(2,1)} %edge_rows.1), channel_id=1, source_target_pairs={{0,2},{2,4},{4,6},{6,8},{8,10},{10,12},{12,14},{14,16},{16,18},{18... | collective-permute-start | bytes 49160 | tf_op jit(solution)/shard_map/ppermute | solution.py:28
  15.7 12.1 %collective-permute-start.21 = (bf16[256,512]{1,0:T(8,128)(2,1)}, bf16[256,512]{1,0:T(8,128)(2,1)S(1)}, u32[]{:S(2)}, u32[]{:S(2)}) collective-permute-start(bf16[256,512]{1,0:T(8,128)(2,1)} %param.27), channel_id=1, source_target_pairs={{0,1},{1,0},{2,3},{3,2},{4,5},{5,4},{6,7},{7,6},{8,9},{9,8},{10,11... | collective-permute-start | bytes 786440 | tf_op jit(solution)/shard_map/ppermute | solution.py:33
  16.1 1.0 copy-start.27
  17.1 0.6 copy-start.28
  17.1 0.7 copy-start.19
  20.5 4.0 %copy-start.14 = (bf16[96,1024]{1,0:T(8,128)(2,1)S(1)}, bf16[96,1024]{1,0:T(8,128)(2,1)}, u32[]{:S(2)}) copy-start(bf16[96,1024]{1,0:T(8,128)(2,1)} %select_ref.1) | copy-start | bytes 589828
  20.5 4.0 %copy-start.22 = (f32[4,1024]{1,0:T(4,128)S(1)}, f32[4,1024]{1,0:T(4,128)}, u32[]{:S(2)}) copy-start(f32[4,1024]{1,0:T(4,128)} %conv_weight_ref.1) | copy-start | bytes 49156
  20.5 7.4 %copy-start.8 = (bf16[256,512]{1,0:T(8,128)(2,1)S(1)}, bf16[256,512]{1,0:T(8,128)(2,1)}, u32[]{:S(2)}) copy-start(bf16[256,512]{1,0:T(8,128)(2,1)} %param.27) | copy-start | bytes 786436
  24.4 3.5 %copy-start = (bf16[1024,1024]{1,0:T(8,128)(2,1)S(1)}, bf16[1024,1024]{1,0:T(8,128)(2,1)}, u32[]{:S(2)}) copy-start(bf16[1024,1024]{1,0:T(8,128)(2,1)} %param.25) | copy-start | bytes 6291460
  27.6 3.5 %collective-permute-start.20 = (f32[96,256]{1,0:T(8,128)S(1)}, f32[96,256]{1,0:T(8,128)S(1)}, u32[]{:S(2)}, u32[]{:S(2)}) collective-permute-start(f32[96,256]{1,0:T(8,128)S(1)} %get-tuple-element.158.selected_ref), channel_id=1, source_target_pairs={{0,1},{1,0},{2,3},{3,2},{4,5},{5,4},{6,7},{7,6},{8,9},{9,8},{10,11... | collective-permute-start | bytes 294920 | tf_op jit(solution)/shard_map/ppermute | solution.py:33
  27.9 3.8 %copy-start.6 = (f32[16,1024]{1,0:T(8,128)S(1)}, f32[16,1024]{1,0:T(8,128)}, u32[]{:S(2)}) copy-start(f32[16,1024]{1,0:T(8,128)} %decay_log_ref.7) | copy-start | bytes 196612
  27.9 3.8 %copy-start.18 = (bf16[64,1024]{1,0:T(8,128)(2,1)S(1)}, bf16[64,1024]{1,0:T(8,128)(2,1)}, u32[]{:S(2)}) copy-start(bf16[64,1024]{1,0:T(8,128)(2,1)} %step_weight_ref.1) | copy-start | bytes 393220
  31.1 0.6 copy-start.11
  41.7 4.2 %collective-permute-start.22 = (bf16[48,1024]{1,0:T(8,128)(2,1)}, bf16[48,1024]{1,0:T(8,128)(2,1)}, u32[]{:S(2)}, u32[]{:S(2)}) collective-permute-start(bf16[48,1024]{1,0:T(8,128)(2,1)} %get-tuple-element.162.own_ref), channel_id=1, source_target_pairs={{0,2},{2,0},{4,6},{6,4},{8,10},{10,8},{12,14},{14,12},{16,18},{18,... | collective-permute-start | bytes 294920 | tf_op jit(solution)/shard_map/ppermute | solution.py:33
  47.6 4.3 %collective-permute-start.23 = (bf16[48,1024]{1,0:T(8,128)(2,1)}, bf16[48,1024]{1,0:T(8,128)(2,1)}, u32[]{:S(2)}, u32[]{:S(2)}) collective-permute-start(bf16[48,1024]{1,0:T(8,128)(2,1)} %get-tuple-element.163.own_ref), channel_id=1, source_target_pairs={{0,4},{2,6},{4,0},{6,2},{8,12},{10,14},{12,8},{14,10},{16,20},{18,... | collective-permute-start | bytes 294920 | tf_op jit(solution)/shard_map/ppermute | solution.py:33
  53.7 6.4 %collective-permute-start.24 = (bf16[16,1024]{1,0:T(8,128)(2,1)}, bf16[16,1024]{1,0:T(8,128)(2,1)S(1)}, u32[]{:S(2)}, u32[]{:S(2)}) collective-permute-start(bf16[16,1024]{1,0:T(8,128)(2,1)} %get-tuple-element.166), channel_id=1, source_target_pairs={{0,8},{2,10},{4,12},{6,14},{8,16},{10,18},{12,20},{14,22},{16,24},... | collective-permute-start | bytes 98312 | tf_op jit(solution)/shard_map/ppermute | solution.py:28
  56.9 15.2 %collective-permute-start.25 = (bf16[16,1024]{1,0:T(8,128)(2,1)}, bf16[16,1024]{1,0:T(8,128)(2,1)S(1)}, u32[]{:S(2)}, u32[]{:S(2)}) collective-permute-start(bf16[16,1024]{1,0:T(8,128)(2,1)} %get-tuple-element.169), channel_id=1, source_target_pairs={{8,0},{10,2},{12,4},{14,6},{16,8},{18,10},{20,12},{22,14},{24,16},... | collective-permute-start | bytes 98312 | tf_op jit(solution)/shard_map/ppermute | solution.py:28
  60.1 0.6 copy-start.24
  72.2 1.0 copy-start.4
  73.1 40.3 %collective-permute-start.2 = (bf16[256,512]{1,0:T(8,128)(2,1)}, bf16[256,512]{1,0:T(8,128)(2,1)S(1)}, u32[]{:S(2)}, u32[]{:S(2)}) collective-permute-start(bf16[256,512]{1,0:T(8,128)(2,1)} %get-tuple-element.86), channel_id=1, source_target_pairs={{0,4},{2,6},{4,0},{6,2},{8,12},{10,14},{12,8},{14,10},{16,20},{18,... | collective-permute-start | bytes 786440 | tf_op jit(solution)/shard_map/cond/branch_1_fun/ppermute | solution.py:33
  96.9 4.1 %collective-permute-start = (f32[96,256]{1,0:T(8,128)}, f32[96,256]{1,0:T(8,128)S(1)}, u32[]{:S(2)}, u32[]{:S(2)}) collective-permute-start(f32[96,256]{1,0:T(8,128)} %get-tuple-element.77.select_grad_ref), channel_id=1, source_target_pairs={{0,1},{1,0},{2,3},{3,2},{4,5},{5,4},{6,7},{7,6},{8,9},{9,8},{10,11... | collective-permute-start | bytes 294920 | tf_op jit(solution)/shard_map/cond/branch_1_fun/ppermute | solution.py:33
  98.2 32.4 %copy-start.30 = (f32[256,1]{0,1:T(1,128)}, f32[256,1]{0,1:T(1,128)S(1)}, u32[]{:S(2)}) copy-start(f32[256,1]{0,1:T(1,128)S(1)} %copy.31) | copy-start | bytes 3076 | tf_op jit(solution)/shard_map/cond
  101.1 0.6 copy-start.21
  105.9 20.3 %copy-start.29 = (s32[256]{0:T(256)S(1)}, s32[256]{0:T(256)}, u32[]{:S(2)}) copy-start(s32[256]{0:T(256)} %get-tuple-element.83.ids_ref) | copy-start | bytes 3076 | tf_op jit(solution)/shard_map/cond
  107.0 23.7 %copy-start.26 = (f32[1024]{0:T(1024)S(1)}, f32[1024]{0:T(1024)}, u32[]{:S(2)}) copy-start(f32[1024]{0:T(1024)} %get-tuple-element.96) | copy-start | bytes 12292 | tf_op jit(solution)/shard_map/cond
  107.0 32.6 %collective-permute-start.3 = (bf16[256,1024]{1,0:T(8,128)(2,1)}, bf16[256,1024]{1,0:T(8,128)(2,1)}, u32[]{:S(2)}, u32[]{:S(2)}) collective-permute-start(bf16[256,1024]{1,0:T(8,128)(2,1)} %get-tuple-element.82), channel_id=1, source_target_pairs={{0,4},{2,6},{4,0},{6,2},{8,12},{10,14},{12,8},{14,10},{16,20},{18,... | collective-permute-start | bytes 1572872 | tf_op jit(solution)/shard_map/cond/branch_1_fun/ppermute | solution.py:33
  108.2 17.3 %collective-permute-start.1 = (f32[8,1024]{1,0:T(8,128)}, f32[8,1024]{1,0:T(8,128)S(1)}, u32[]{:S(2)}, u32[]{:S(2)}) collective-permute-start(f32[8,1024]{1,0:T(8,128)} %get-tuple-element.85), channel_id=1, source_target_pairs={{2,0},{4,2},{6,4},{8,6},{10,8},{12,10},{14,12},{16,14},{18,16},{20... | collective-permute-start | bytes 98312 | tf_op jit(solution)/shard_map/cond/branch_1_fun/ppermute | solution.py:28
  113.4 12.1 %copy-start.10 = (bf16[256,512]{1,0:T(8,128)(2,1)}, bf16[256,512]{1,0:T(8,128)(2,1)S(1)}, u32[]{:S(2)}) copy-start(bf16[256,512]{1,0:T(8,128)(2,1)S(1)} %collective-permute-done.2.wait_ref) | copy-start | bytes 786436 | tf_op jit(solution)/shard_map/cond
  114.2 26.5 %collective-permute-start.7 = (bf16[512,256]{1,0:T(8,128)(2,1)S(1)}, bf16[512,256]{1,0:T(8,128)(2,1)S(1)}, u32[]{:S(2)}, u32[]{:S(2)}) collective-permute-start(bf16[512,256]{1,0:T(8,128)(2,1)S(1)} %get-tuple-element.230), channel_id=1, source_target_pairs={{0,2},{2,0},{4,6},{6,4},{8,10},{10,8},{12,14},{14,12},{16,18},{18,... | collective-permute-start | bytes 786440 | tf_op jit(solution)/shard_map/cond/branch_1_fun/ppermute | solution.py:33
  125.5 0.6 copy-start.25
  129.8 5.5 %collective-permute-start.4 = (bf16[128,1024]{1,0:T(8,128)(2,1)}, bf16[128,1024]{1,0:T(8,128)(2,1)S(1)}, u32[]{:S(2)}, u32[]{:S(2)}) collective-permute-start(bf16[128,1024]{1,0:T(8,128)(2,1)} %get-tuple-element.90), channel_id=1, source_target_pairs={{0,2},{2,0},{4,6},{6,4},{8,10},{10,8},{12,14},{14,12},{16,18},{18,... | collective-permute-start | bytes 786440 | tf_op jit(solution)/shard_map/cond/branch_1_fun/ppermute | solution.py:33
  130.7 7.3 %copy-start.12 = (bf16[16,1024]{1,0:T(8,128)(2,1)S(1)}, bf16[16,1024]{1,0:T(8,128)(2,1)}, u32[]{:S(2)}) copy-start(bf16[16,1024]{1,0:T(8,128)(2,1)} %patched.1.wait_ref) | copy-start | bytes 98308 | tf_op jit(solution)/shard_map/cond
  135.0 4.0 %collective-permute-start.6 = (f32[1,1280]{1,0:T(1,128)S(1)}, f32[1,1280]{1,0:T(1,128)S(1)}, u32[]{:S(2)}, u32[]{:S(2)}) collective-permute-start(f32[1,1280]{1,0:T(1,128)S(1)} %pad_maximum_fusion.6), channel_id=1, source_target_pairs={{0,1},{1,0},{2,3},{3,2},{4,5},{5,4},{6,7},{7,6},{8,9},{9,8},{10,11... | collective-permute-start | bytes 15368 | tf_op jit(solution)/shard_map/cond/branch_1_fun/ppermute | solution.py:33
  135.4 0.7 copy-start.20
  138.0 11.4 %copy-start.31 = (f32[256,1]{0,1:T(1,128)S(1)}, f32[256,1]{0,1:T(1,128)}, u32[]{:S(2)}) copy-start(f32[256,1]{0,1:T(1,128)} %copy-done.30) | copy-start | bytes 3076 | tf_op jit(solution)/shard_map/cond
  138.9 8.1 %collective-permute-start.5 = (bf16[80,1024]{1,0:T(8,128)(2,1)S(1)}, bf16[80,1024]{1,0:T(8,128)(2,1)S(1)}, u32[]{:S(2)}, u32[]{:S(2)}) collective-permute-start(bf16[80,1024]{1,0:T(8,128)(2,1)S(1)} %pad_maximum_fusion.4), channel_id=1, source_target_pairs={{0,4},{2,6},{4,0},{6,2},{8,12},{10,14},{12,8},{14,10},{16,20},{18,... | collective-permute-start | bytes 491528 | tf_op jit(solution)/shard_map/cond/branch_1_fun/ppermute | solution.py:33
  140.7 9.6 %copy-start.23 = (f32[1,1280]{1,0:T(1,128)S(1)}, f32[1,1280]{1,0:T(1,128)}, u32[]{:S(2)}) copy-start(f32[1,1280]{1,0:T(1,128)} %fusion.21.refs_1_) | copy-start | bytes 15364 | tf_op jit(solution)/shard_map/cond
  140.7 6.3 %copy-start.7 = (bf16[512,256]{1,0:T(8,128)(2,1)}, bf16[512,256]{1,0:T(8,128)(2,1)S(1)}, u32[]{:S(2)}) copy-start(bf16[512,256]{1,0:T(8,128)(2,1)S(1)} %collective-permute-done.7.refs_2_.far_normed_ref) | copy-start | bytes 786436 | tf_op jit(solution)/shard_map/cond
  147.0 0.7 copy-start.13
  148.5 3.3 %copy-start.2 = (bf16[512,1024]{1,0:T(8,128)(2,1)}, bf16[512,1024]{1,0:T(8,128)(2,1)S(1)}, u32[]{:S(2)}) copy-start(bf16[512,1024]{1,0:T(8,128)(2,1)S(1)} %pad_maximum_fusion.ours_ref) | copy-start | bytes 3145732 | tf_op jit(solution)/shard_map/cond
  148.5 3.3 %collective-permute-start.8 = (bf16[512,1024]{1,0:T(8,128)(2,1)S(1)}, bf16[512,1024]{1,0:T(8,128)(2,1)}, u32[]{:S(2)}, u32[]{:S(2)}) collective-permute-start(bf16[512,1024]{1,0:T(8,128)(2,1)S(1)} %pad_maximum_fusion.ours_ref), channel_id=1, source_target_pairs={{0,2},{2,0},{4,6},{6,4},{8,10},{10,8},{12,14},{14,12},{16,18},{18,... | collective-permute-start | bytes 3145736 | tf_op jit(solution)/shard_map/cond/branch_1_fun/ppermute | solution.py:33
  155.2 2.7 %copy-start.1 = (bf16[1024,1024]{1,0:T(8,128)(2,1)S(1)}, bf16[1024,1024]{1,0:T(8,128)(2,1)}, u32[]{:S(2)}) copy-start(bf16[1024,1024]{1,0:T(8,128)(2,1)} %get-tuple-element.106) | copy-start | bytes 6291460 | tf_op jit(solution)/shard_map/cond
  155.2 21.5 %copy-start.3 = (f32[80,1024]{1,0:T(8,128)S(1)}, f32[80,1024]{1,0:T(8,128)}, u32[]{:S(2)}) copy-start(f32[80,1024]{1,0:T(8,128)} %get-tuple-element.99.refs_1_) | copy-start | bytes 983044 | tf_op jit(solution)/shard_map/cond
  155.3 8.2 %collective-permute-start.9 = (bf16[80,1024]{1,0:T(8,128)(2,1)}, bf16[80,1024]{1,0:T(8,128)(2,1)S(1)}, u32[]{:S(2)}, u32[]{:S(2)}) collective-permute-start(bf16[80,1024]{1,0:T(8,128)(2,1)} %get-tuple-element.100), channel_id=1, source_target_pairs={{0,8},{2,10},{4,12},{6,14},{8,0},{10,2},{12,4},{14,6},{16,24},{18,... | collective-permute-start | bytes 491528 | tf_op jit(solution)/shard_map/cond/branch_1_fun/ppermute | solution.py:33
  156.5 11.1 %collective-permute-start.10 = (bf16[80,1024]{1,0:T(8,128)(2,1)}, bf16[80,1024]{1,0:T(8,128)(2,1)S(1)}, u32[]{:S(2)}, u32[]{:S(2)}) collective-permute-start(bf16[80,1024]{1,0:T(8,128)(2,1)} %get-tuple-element.101), channel_id=1, source_target_pairs={{0,16},{2,18},{4,20},{6,22},{8,24},{10,26},{12,28},{14,30},{16,0},... | collective-permute-start | bytes 491528 | tf_op jit(solution)/shard_map/cond/branch_1_fun/ppermute | solution.py:33
  156.8 20.0 %collective-permute-start.11 = (bf16[80,1024]{1,0:T(8,128)(2,1)}, bf16[80,1024]{1,0:T(8,128)(2,1)S(1)}, u32[]{:S(2)}, u32[]{:S(2)}) collective-permute-start(bf16[80,1024]{1,0:T(8,128)(2,1)} %get-tuple-element.102), channel_id=1, source_target_pairs={{0,24},{2,26},{4,28},{6,30},{8,16},{10,18},{12,20},{14,22},{16,8},... | collective-permute-start | bytes 491528 | tf_op jit(solution)/shard_map/cond/branch_1_fun/ppermute | solution.py:33
  159.7 17.5 %copy-start.5 = (f32[256,512]{1,0:T(8,128)S(1)}, f32[256,512]{1,0:T(8,128)}, u32[]{:S(2)}) copy-start(f32[256,512]{1,0:T(8,128)} %after.6) | copy-start | bytes 1572868 | tf_op jit(solution)/shard_map/cond
  176.9 5.7 %collective-permute-start.14 = (bf16[80,1024]{1,0:T(8,128)(2,1)S(1)}, bf16[80,1024]{1,0:T(8,128)(2,1)S(1)}, u32[]{:S(2)}, u32[]{:S(2)}) collective-permute-start(bf16[80,1024]{1,0:T(8,128)(2,1)S(1)} %pad_maximum_fusion.5), channel_id=1, source_target_pairs={{0,8},{2,10},{4,12},{6,14},{8,0},{10,2},{12,4},{14,6},{16,24},{18,... | collective-permute-start | bytes 491528 | tf_op jit(solution)/shard_map/cond/branch_1_fun/ppermute | solution.py:33
  177.0 26.4 %copy-start.9 = (bf16[256,512]{1,0:T(8,128)(2,1)S(1)}, bf16[256,512]{1,0:T(8,128)(2,1)}, u32[]{:S(2)}) copy-start(bf16[256,512]{1,0:T(8,128)(2,1)} %get-tuple-element.107) | copy-start | bytes 786436 | tf_op jit(solution)/shard_map/cond
  177.1 26.4 %collective-permute-start.15 = (f32[256,512]{1,0:T(8,128)S(1)}, f32[256,512]{1,0:T(8,128)S(1)}, u32[]{:S(2)}, u32[]{:S(2)}) collective-permute-start(f32[256,512]{1,0:T(8,128)S(1)} %slice_select_fusion.1), channel_id=1, source_target_pairs={{0,1},{1,0},{2,3},{3,2},{4,5},{5,4},{6,7},{7,6},{8,9},{9,8},{10,11... | collective-permute-start | bytes 1572872 | tf_op jit(solution)/shard_map/cond/branch_1_fun/ppermute | solution.py:33
  177.2 26.2 %collective-permute-start.16 = (f32[256,512]{1,0:T(8,128)S(1)}, f32[256,512]{1,0:T(8,128)S(1)}, u32[]{:S(2)}, u32[]{:S(2)}) collective-permute-start(f32[256,512]{1,0:T(8,128)S(1)} %copy-done.5), channel_id=1, source_target_pairs={{0,1},{1,0},{2,3},{3,2},{4,5},{5,4},{6,7},{7,6},{8,9},{9,8},{10,11... | collective-permute-start | bytes 1572872 | tf_op jit(solution)/shard_map/cond/branch_1_fun/ppermute | solution.py:33
  178.6 8.7 %collective-permute-start.13 = (bf16[80,1024]{1,0:T(8,128)(2,1)S(1)}, bf16[80,1024]{1,0:T(8,128)(2,1)S(1)}, u32[]{:S(2)}, u32[]{:S(2)}) collective-permute-start(bf16[80,1024]{1,0:T(8,128)(2,1)S(1)} %pad_maximum_fusion.5), channel_id=1, source_target_pairs={{0,16},{2,18},{4,20},{6,22},{8,24},{10,26},{12,28},{14,30},{16,0},... | collective-permute-start | bytes 491528 | tf_op jit(solution)/shard_map/cond/branch_1_fun/ppermute | solution.py:33
  178.6 23.7 %collective-permute-start.12 = (bf16[80,1024]{1,0:T(8,128)(2,1)S(1)}, bf16[80,1024]{1,0:T(8,128)(2,1)S(1)}, u32[]{:S(2)}, u32[]{:S(2)}) collective-permute-start(bf16[80,1024]{1,0:T(8,128)(2,1)S(1)} %pad_maximum_fusion.5), channel_id=1, source_target_pairs={{0,24},{2,26},{4,28},{6,30},{8,16},{10,18},{12,20},{14,22},{16,8},... | collective-permute-start | bytes 491528 | tf_op jit(solution)/shard_map/cond/branch_1_fun/ppermute | solution.py:33
  204.5 12.7 %collective-permute-start.27 = (bf16[320,1024]{1,0:T(8,128)(2,1)}, bf16[320,1024]{1,0:T(8,128)(2,1)S(1)}, u32[]{:S(2)}, u32[]{:S(2)}) collective-permute-start(bf16[320,1024]{1,0:T(8,128)(2,1)} %get-tuple-element.181.rest_0_), channel_id=1, source_target_pairs={{0,4},{2,6},{4,0},{6,2},{8,12},{10,14},{12,8},{14,10},{16,20},{18,... | collective-permute-start | bytes 1966088 | tf_op jit(solution)/shard_map/ppermute | solution.py:33
  204.7 17.1 %collective-permute-start.26 = (bf16[320,1024]{1,0:T(8,128)(2,1)}, bf16[320,1024]{1,0:T(8,128)(2,1)S(1)}, u32[]{:S(2)}, u32[]{:S(2)}) collective-permute-start(bf16[320,1024]{1,0:T(8,128)(2,1)} %get-tuple-element.181.rest_0_), channel_id=1, source_target_pairs={{0,2},{2,0},{4,6},{6,4},{8,10},{10,8},{12,14},{14,12},{16,18},{18,... | collective-permute-start | bytes 1966088 | tf_op jit(solution)/shard_map/ppermute | solution.py:33
  217.2 6.4 %copy-start.15 = (bf16[320,1024]{1,0:T(8,128)(2,1)}, bf16[320,1024]{1,0:T(8,128)(2,1)S(1)}, u32[]{:S(2)}) copy-start(bf16[320,1024]{1,0:T(8,128)(2,1)S(1)} %collective-permute-done.27.rest_2_) | copy-start | bytes 1966084
  217.2 6.3 %collective-permute-start.28 = (bf16[320,1024]{1,0:T(8,128)(2,1)S(1)}, bf16[320,1024]{1,0:T(8,128)(2,1)S(1)}, u32[]{:S(2)}, u32[]{:S(2)}) collective-permute-start(bf16[320,1024]{1,0:T(8,128)(2,1)S(1)} %collective-permute-done.27.rest_2_), channel_id=1, source_target_pairs={{0,2},{2,0},{4,6},{6,4},{8,10},{10,8},{12,14},{14,12},{16,18},{18,... | collective-permute-start | bytes 1966088 | tf_op jit(solution)/shard_map/ppermute | solution.py:33
  221.9 1.7 copy-start.16
  223.6 0.9 copy-start.17
Sparse Core Ops, SparseCore 0:
  72.3 142.3 all-reduce.2

commit v22 on v20

--- a/solution.py
+++ b/solution.py
@@ -143,12 +143,9 @@
     conv_bias_ref,
     select_ref,
     mask_ref,
-    cot_ref,
-    other_cot_ref,
     convolved_ref,
     act_ref,
     selected_ref,
-    whole_cot_ref,
     inner,
 ):
     rows = act_ref.shape[0]
@@ -167,17 +164,13 @@
     @pl.when(pl.program_id(0) == 0)
     def _():
         selected_ref[...] = part
-        half = cot_ref.shape[1]
-        right = lax.axis_index("narrow") == 1
-        whole_cot_ref[:, :half] = jnp.where(right, other_cot_ref[...], cot_ref[...])
-        whole_cot_ref[:, half:] = jnp.where(right, cot_ref[...], other_cot_ref[...])
 
     @pl.when(pl.program_id(0) > 0)
     def _():
         selected_ref[...] += part
 
 
-def convolve(projected, conv_weight, conv_bias, select_weight, masks, cot, other_cot):
+def convolve(projected, conv_weight, conv_bias, select_weight, masks):
     parts, extended, width = projected.shape
     rows = extended - halo
     taps = conv_weight.shape[0]
@@ -192,20 +185,12 @@
             column_spec(1),
             column_spec(columns),
             whole_spec(rows, masks.shape[1]),
-            whole_spec(*cot.shape),
-            whole_spec(*cot.shape),
         ],
-        [
-            column_spec(rows),
-            column_spec(rows),
-            whole_spec(columns, rows),
-            whole_spec(rows, 2 * cot.shape[1]),
-        ],
+        [column_spec(rows), column_spec(rows), whole_spec(columns, rows)],
         [
             jax.ShapeDtypeStruct((rows, width), f32),
             jax.ShapeDtypeStruct((rows, width), bf16),
             jax.ShapeDtypeStruct((columns, rows), f32),
-            jax.ShapeDtypeStruct((rows, 2 * cot.shape[1]), bf16),
         ],
         [pltpu.VMEM((extended, scan_width), f32)],
         projected,
@@ -213,8 +198,6 @@
         conv_bias,
         select_weight,
         masks,
-        cot,
-        other_cot,
     )
 
 
@@ -1171,6 +1154,11 @@
     count = decay_log.shape[0]
     right_half = lax.axis_index("narrow") == 1
 
+    def both_halves(own, other):
+        return jnp.concatenate(
+            [jnp.where(right_half, other, own), jnp.where(right_half, own, other)], axis=1
+        )
+
     other_tokens = swapped(tokens, "narrow", 1)
     other_cot = swapped(cotangent, "narrow", 1)
     edge, other_edge = to_next_both(edge_rows_of(segment_ids, tokens))
@@ -1181,10 +1169,11 @@
     projected = jnp.einsum(
         "td,dce->cte", normed_ext, in_weight, preferred_element_type=f32
     ).astype(bf16)
-    convolved, act, selected, cot_whole = convolve(
-        projected, conv_weight, conv_bias[None], select_weight, masks, cotangent, other_cot
+    convolved, act, selected = convolve(
+        projected, conv_weight, conv_bias[None], select_weight, masks
     )
     other_selected = swapped(selected, "narrow", 1)
+    cot_whole = both_halves(cotangent, other_cot)
     gated_grad = lax.dot_general(
         cot_whole, out_weight, contract_last, preferred_element_type=f32
     )
@@ -1264,15 +1253,17 @@
         normed_part = jnp.einsum(
             "cte,dce->td", jnp.stack([inner_grad, gate_grad]), in_weight, preferred_element_type=f32
         )
-        inverse_then = after(inverse, send)
-        gain_part = jnp.sum(normed_part * whole * inverse_then, axis=0, keepdims=True)
+        gain_part = jnp.sum(normed_part * whole * inverse, axis=0, keepdims=True)
         row_part = jnp.sum(normed_part * norm_gain * whole, axis=1)[None]
         first_bits, *more_bits = group_bits(2)
-        gain_sum = gain_part + swapped(gain_part, "narrow", 1)
+        narrow_sums = jnp.concatenate([gain_part, row_part], axis=1)
+        narrow_sums = narrow_sums + swapped(narrow_sums, "narrow", 1)
+        gain_sum = narrow_sums[:, : 2 * features]
         for bit in (bit for bits in more_bits for bit in bits):
             gain_sum = gain_sum + swapped(gain_sum, "wide", bit)
-        row_theirs = swapped(row_part, "narrow", 1)
-        near = after(near, gain_part, smalls[1])
+        normed_mine, normed_other = narrow_halves(normed_part)
+        normed_theirs = swapped(normed_other, "narrow", 1)
+        near = after(near, narrow_sums, smalls[1], normed_theirs)
         far = swapped(jnp.concatenate([inner_grad, near]), "wide", 1)
         keep, *sends = inner_quarter(
             (wide_place >> 2 & 3)[None],
@@ -1283,13 +1274,11 @@
             smalls,
             [],
         )
-        normed_mine, normed_other = narrow_halves(normed_part)
-        normed_theirs = swapped(after(normed_other, keep), "narrow", 1)
         out_part = jnp.dot(after(gated, keep), out_weight, preferred_element_type=f32)
         out_mine, out_other = narrow_halves(out_part)
         out_theirs = swapped(out_other, "narrow", 1)
         layer_out = (tokens.astype(f32) + (out_mine + out_theirs)).astype(bf16)
-        row_sum = (row_part + row_theirs).reshape(rows, 1)
+        row_sum = narrow_sums[:, 2 * features :].reshape(rows, 1)
         gain_mine = jnp.where(right_half, norm_gain[features:], norm_gain[:features])
         whole_grad = inverse * (gain_mine * (normed_mine + normed_theirs)) - tokens.astype(f32) * (
             inverse * inverse * inverse

time: 231 us -> 232 us (level)
  waiting for transfers between devices: 63.6 us -> 69.9 us
  matrix products: 12.2 us -> 9.79 us
    ppermute x26 -> x25, waiting for transfers between devices: 61.3 us -> 68.1 us  [swapped(): return lax.ppermute(array, axis, [(i, i ^ bit) for i in range(peers)])]
    ppermute x26 -> x25, starting transfers between devices: 35.4 us -> 33.4 us  [swapped(): return lax.ppermute(array, axis, [(i, i ^ bit) for i in range(peers)])]
  transfers between devices with their start and end apart: 32 -> 31, of which waited for: 15 -> 14; matrix products, arithmetic and copies ran while one was open for 8% -> 8% of each run, Pallas kernels for 23% -> 24%
where the time goes in v22:
time: 232 us; the launch traced here: 231 us
  Pallas kernels  77 us (33%)
  waiting for transfers between devices  69.9 us (30%)
  starting transfers between devices  46.5 us (20%)
  between operations  14.3 us (6%)
  matrix products  9.79 us (4%)
  other arithmetic  7.18 us (3%)
  local copies, waits for them, and re-layouts  6.26 us (3%)
    ppermute x25, waiting for transfers between devices, swapped(): return lax.ppermute(array, axis, [(i, i ^ bit) for i in range(peers)])  68.1 us
    pallas_call x5, Pallas kernels, call(): pl.pallas_call(kernel, grid=(width // scan_width,), in_specs=in_specs, ou...  51.9 us
    ppermute x25, starting transfers between devices, swapped(): return lax.ppermute(array, axis, [(i, i ^ bit) for i in range(peers)])  33.4 us
    ppermute x4, starting transfers between devices, passed_along(): return lax.ppermute(array, axis, pairs)  11.7 us
    pallas_call x1, Pallas kernels, joined(): pl.pallas_call(functools.partial(join_kernel, small_rows=small_rows), gri...  8.91 us
  transfers between devices with their start and end apart: 31, of which 14 were waited for; matrix products, arithmetic and copies ran while one was open for 8% of the time, Pallas kernels for 24%

profile of v22, /device:TPU:0, one launch (start us, length us, event | category | flops | bytes accessed | tf_op | source)
XLA Modules:
  0.0 231.2 jit_solution(15610398215765237012)
XLA Ops:
  7.2 3.0 %collective-permute-start.18 = (bf16[256,512]{1,0:T(8,128)(2,1)}, bf16[256,512]{1,0:T(8,128)(2,1)S(1)}, u32[]{:S(2)}, u32[]{:S(2)}) collective-permute-start(bf16[256,512]{1,0:T(8,128)(2,1)} %own_ref.1), channel_id=1, source_target_pairs={{0,1},{1,0},{2,3},{3,2},{4,5},{5,4},{6,7},{7,6},{8,9},{9,8},{10,11... | collective-permute-start | bytes 786440 | tf_op jit(solution)/shard_map/ppermute | solution.py:33
  10.3 1.4 edge_rows.1
  11.6 1.3 collective-permute-start.20
  13.0 4.0 %collective-permute-start.19 = (bf16[16,512]{1,0:T(8,128)(2,1)}, bf16[16,512]{1,0:T(8,128)(2,1)S(1)}, u32[]{:S(2)}, u32[]{:S(2)}) collective-permute-start(bf16[16,512]{1,0:T(8,128)(2,1)} %edge_rows.1), channel_id=1, source_target_pairs={{0,2},{2,4},{4,6},{6,8},{8,10},{10,12},{12,14},{14,16},{16,18},{18... | collective-permute-start | bytes 49160 | tf_op jit(solution)/shard_map/ppermute | solution.py:28
  17.0 1.6 collective-permute-start.22
  19.3 2.3 normalized.1
  21.6 4.0 %fusion.27.inner_ref.gate_ref = bf16[2,272,1024]{2,1,0:T(8,128)(2,1)S(1)} fusion(bf16[1024,2,1024]{2,1,0:T(2,128)(2,1)} %param.17, bf16[272,1024]{1,0:T(8,128)(2,1)} %get-tuple-element.151), kind=kOutput, calls=%fused_computation.50 | convolution fusion | flops 1141407744 | bytes 5865472 | tf_op jit(solution)/shard_map/td,dce->cte/dot_general | solution.py:1169
  25.6 3.1 %convolve.1 = (f32[256,1024]{1,0:T(8,128)}, bf16[256,1024]{1,0:T(8,128)(2,1)S(1)}, f32[96,256]{1,0:T(8,128)S(1)}) custom-call(bf16[2,272,1024]{2,1,0:T(8,128)(2,1)S(1)} %fusion.27.inner_ref.gate_ref, f32[4,1024]{1,0:T(4,128)S(1)} %copy-done.31, f32[1,1024]{1,0:T(1,128)} %bitcast.42, bf16[96,1024]{1,0:T(8,128)(2,1)S(1)} %copy-done.18, ...), custom_call_target="tpu_custom_call" | custom-call | flops 1 | bytes 1 | tf_op jit(solution)/shard_map/convolve/pallas_call | solution.py:127
  28.7 0.9 collective-permute-start.21
  29.7 0.7 fusion.31.gated_grad_ref
  30.5 2.8 %collective-permute-done.21.other_ref = f32[96,256]{1,0:T(8,128)S(1)} collective-permute-done((f32[96,256]{1,0:T(8,128)S(1)}, f32[96,256]{1,0:T(8,128)S(1)}, u32[]{:S(2)}, u32[]{:S(2)}) %collective-permute-start.21) | collective-permute-done | bytes 98336 | tf_op jit(solution)/shard_map/ppermute | solution.py:33
  33.3 10.0 %scan_ends.1 = (f32[256,1024]{1,0:T(8,128)}, f32[256,1024]{1,0:T(8,128)}, bf16[48,1024]{1,0:T(8,128)(2,1)}) custom-call(f32[96,256]{1,0:T(8,128)S(1)} %get-tuple-element.153.selected_ref, f32[96,256]{1,0:T(8,128)S(1)} %collective-permute-done.21.other_ref, bf16[64,1024]{1,0:T(8,128)(2,1)S(1)} %copy-done.23, f32[1,1024]{1,0:T(1,128)} %bitcast.43, ...), custom_call_target="tpu_custom_call" | custom-call | flops 1 | bytes 1 | tf_op jit(solution)/shard_map/scan_ends/pallas_call | solution.py:127
  43.4 1.6 collective-permute-done.23.other_ref
  45.0 1.7 carry_round.2
  46.8 1.7 collective-permute-start.24
  48.5 3.5 %collective-permute-done.24.other_ref = bf16[48,1024]{1,0:T(8,128)(2,1)} collective-permute-done((bf16[48,1024]{1,0:T(8,128)(2,1)}, bf16[48,1024]{1,0:T(8,128)(2,1)}, u32[]{:S(2)}, u32[]{:S(2)}) %collective-permute-start.24) | collective-permute-done | bytes 98336 | tf_op jit(solution)/shard_map/ppermute | solution.py:33
  51.9 1.8 carry_round.3
  53.7 4.6 %collective-permute-start.25 = (bf16[16,1024]{1,0:T(8,128)(2,1)}, bf16[16,1024]{1,0:T(8,128)(2,1)S(1)}, u32[]{:S(2)}, u32[]{:S(2)}) collective-permute-start(bf16[16,1024]{1,0:T(8,128)(2,1)} %get-tuple-element.161), channel_id=1, source_target_pairs={{0,8},{2,10},{4,12},{6,14},{8,16},{10,18},{12,20},{14,22},{16,24},... | collective-permute-start | bytes 98312 | tf_op jit(solution)/shard_map/ppermute | solution.py:28
  58.3 1.5 collective-permute-start.26
  59.8 1.9 pad_maximum_fusion.6.cot_ref
  62.3 11.3 %scan_forward.1 = (bf16[256,1024]{1,0:T(8,128)(2,1)}, bf16[256,1024]{1,0:T(8,128)(2,1)}, bf16[1024,1024]{1,0:T(8,128)(2,1)}, bf16[1024,1024]{1,0:T(8,128)(2,1)}, f32[16,1024]{1,0:T(8,128)}) custom-call(f32[96,256]{1,0:T(8,128)S(1)} %get-tuple-element.153.selected_ref, f32[96,256]{1,0:T(8,128)} %copy-done.17, f32[256,1024]{1,0:T(8,128)} %get-tuple-element.156.step_ref, ...), custom_call_target="tpu_custom_call" | custom-call | flops 1 | bytes 1 | tf_op jit(solution)/shard_map/scan_forward/pallas_call | solution.py:127
  73.6 124.7 %conditional.1 = (bf16[320,1024]{1,0:T(8,128)(2,1)}, bf16[256,512]{1,0:T(8,128)(2,1)}, bf16[256,512]{1,0:T(8,128)(2,1)}) conditional(s32[]{:T(128)} %convert_element_type.41, () %tuple.16, (s32[]{:T(128)}, f32[1024]{0:T(1024)}, f32[96,256]{1,0:T(8,128)S(1)}, f32[96,256]{1,0:T(8,128)}, f32[256,1024]{1,0:T(8,128)}, /*index=5*/f32[256,1024]{1,0:T(8,128)}, ...), branch_computations={%region_0.1_spmd, %region_1.4_spmd} | conditional | flops 1621778176 | bytes 85409512 | solution.py:1301
  73.6 23.5 %scan_backward.1 = (f32[256,1024]{1,0:T(8,128)}, f32[96,256]{1,0:T(8,128)}, f32[82,1024]{1,0:T(8,128)}) custom-call(f32[96,256]{1,0:T(8,128)S(1)} %get-tuple-element.62.selected_ref, f32[96,256]{1,0:T(8,128)} %get-tuple-element.63.other_ref, f32[256,1024]{1,0:T(8,128)} %get-tuple-element.64.step_pre_ref, f32[256,1024]{1,0:T(8,128)} %get-tuple-element.65.step_ref, ...), custom_call_target="tpu_custom_call" | custom-call | flops 1 | bytes 1 | tf_op jit(solution)/shard_map/cond/branch_1_fun/scan_backward/pallas_call | solution.py:127
  97.2 1.5 collective-permute-start
  98.7 0.8 constant_dynamic-slice_fusion
  99.5 0.7 collective-permute-start.3
  100.2 1.4 collective-permute-start.2
  102.2 4.0 %convolve_grad.1 = (bf16[256,1024]{1,0:T(8,128)(2,1)}, f32[8,1024]{1,0:T(8,128)}, f32[8,1024]{1,0:T(8,128)}, f32[101,1024]{1,0:T(8,128)}) custom-call(f32[96,256]{1,0:T(8,128)} %get-tuple-element.76.select_grad_ref.refs_1_, f32[96,256]{1,0:T(8,128)} %collective-permute-done.other_ref, bf16[96,1024]{1,0:T(8,128)(2,1)S(1)} %copy-done.19, ...), custom_call_target="tpu_custom_call" | custom-call | flops 1 | bytes 1 | tf_op jit(solution)/shard_map/cond/branch_1_fun/convolve_grad/pallas_call | solution.py:127
  106.2 1.6 collective-permute-start.1
  107.9 1.7 collective-permute-done.1.next_ref
  110.4 1.4 patched.1.wait_ref.own_ref
  111.9 1.4 collective-permute-start.5
  113.2 2.2 small_halves.1
  115.4 3.1 %collective-permute-start.7 = (bf16[128,1024]{1,0:T(8,128)(2,1)}, bf16[128,1024]{1,0:T(8,128)(2,1)S(1)}, u32[]{:S(2)}, u32[]{:S(2)}) collective-permute-start(bf16[128,1024]{1,0:T(8,128)(2,1)} %get-tuple-element.93), channel_id=1, source_target_pairs={{0,2},{2,0},{4,6},{6,4},{8,10},{10,8},{12,14},{14,12},{16,18},{18,... | collective-permute-start | bytes 786440 | tf_op jit(solution)/shard_map/cond/branch_1_fun/ppermute | solution.py:33
  118.5 4.4 %fusion.6 = (f32[1024]{0:T(1024)S(1)}, f32[256]{0:T(256)S(1)}, f32[256,1024]{1,0:T(8,128)S(1)}) fusion(bf16[256,1024]{1,0:T(8,128)(2,1)S(1)} %copy-done.38, f32[256]{0:T(256)S(1)} %bitcast.40, f32[1024]{0:T(1024)S(1)} %copy-done.35, bf16[1024,2,1024]{2,1,0:T(2,128)(2,1)} %get-tuple-element.206, bf16[1,256,1024]{2,1,0:T(8,128)(2,1)} %bitcast.48, ...), kind=kOutput, calls=%fused_computation.6 | convolution fusion | flops 1076099840 | bytes 6825984 | tf_op jit(solution)/shard_map/cond/branch_1_fun/cte,dce->td/dot_general | solution.py:1253
  123.0 1.4 collective-permute-start.9
  124.5 0.7 collective-permute-start.6
  125.1 0.7 copy-done.29
  125.9 1.9 folded.1
  127.9 9.1 %collective-permute-done.6 = f32[1,1280]{1,0:T(1,128)S(1)} collective-permute-done((f32[1,1280]{1,0:T(1,128)S(1)}, f32[1,1280]{1,0:T(1,128)S(1)}, u32[]{:S(2)}, u32[]{:S(2)}) %collective-permute-start.6) | collective-permute-done | bytes 5152 | tf_op jit(solution)/shard_map/cond/branch_1_fun/ppermute | solution.py:33
  137.7 0.6 copy-done.24
  138.5 0.8 copy-done.3
  139.3 2.1 pad_maximum_fusion
  141.5 2.9 %collective-permute-done.10.far_ref = bf16[512,1024]{1,0:T(8,128)(2,1)} collective-permute-done((bf16[512,1024]{1,0:T(8,128)(2,1)}, bf16[512,1024]{1,0:T(8,128)(2,1)}, u32[]{:S(2)}, u32[]{:S(2)}) %collective-permute-start.10) | collective-permute-done | bytes 1048608 | tf_op jit(solution)/shard_map/cond/branch_1_fun/ppermute | solution.py:33
  144.5 3.6 %inner_quarter.1 = (f32[80,1024]{1,0:T(8,128)}, bf16[80,1024]{1,0:T(8,128)(2,1)}, bf16[80,1024]{1,0:T(8,128)(2,1)}, bf16[80,1024]{1,0:T(8,128)(2,1)}) custom-call(s32[1]{0:T(128)} %bitcast.place_ref, bf16[256,1024]{1,0:T(8,128)(2,1)} %patched.1.wait_ref.own_ref, bf16[256,1024]{1,0:T(8,128)(2,1)} %after.5.near_ref, ...), custom_call_target="tpu_custom_call" | custom-call | flops 1 | bytes 1 | tf_op jit(solution)/shard_map/cond/branch_1_fun/inner_quarter/pallas_call | solution.py:1000
  148.0 1.5 collective-permute-start.11
  149.6 1.1 collective-permute-start.12
  150.7 1.8 collective-permute-start.13
  152.4 0.7 fusion.32
  153.1 5.8 %collective-permute-done.11 = bf16[80,1024]{1,0:T(8,128)(2,1)S(1)} collective-permute-done((bf16[80,1024]{1,0:T(8,128)(2,1)}, bf16[80,1024]{1,0:T(8,128)(2,1)S(1)}, u32[]{:S(2)}, u32[]{:S(2)}) %collective-permute-start.11) | collective-permute-done | bytes 163872 | tf_op jit(solution)/shard_map/cond/branch_1_fun/ppermute | solution.py:33
  158.9 6.0 %collective-permute-done.12 = bf16[80,1024]{1,0:T(8,128)(2,1)S(1)} collective-permute-done((bf16[80,1024]{1,0:T(8,128)(2,1)}, bf16[80,1024]{1,0:T(8,128)(2,1)S(1)}, u32[]{:S(2)}, u32[]{:S(2)}) %collective-permute-start.12) | collective-permute-done | bytes 163872 | tf_op jit(solution)/shard_map/cond/branch_1_fun/ppermute | solution.py:33
  165.1 6.5 %collective-permute-start.16 = (bf16[80,1024]{1,0:T(8,128)(2,1)S(1)}, bf16[80,1024]{1,0:T(8,128)(2,1)S(1)}, u32[]{:S(2)}, u32[]{:S(2)}) collective-permute-start(bf16[80,1024]{1,0:T(8,128)(2,1)S(1)} %pad_maximum_fusion.4), channel_id=1, source_target_pairs={{0,8},{2,10},{4,12},{6,14},{8,0},{10,2},{12,4},{14,6},{16,24},{18,... | collective-permute-start | bytes 491528 | tf_op jit(solution)/shard_map/cond/branch_1_fun/ppermute | solution.py:33
  171.8 1.5 collective-permute-start.17
  173.3 1.8 collective-permute-start.15
  175.1 1.4 collective-permute-start.14
  176.5 4.7 %collective-permute-done.16 = bf16[80,1024]{1,0:T(8,128)(2,1)S(1)} collective-permute-done((bf16[80,1024]{1,0:T(8,128)(2,1)S(1)}, bf16[80,1024]{1,0:T(8,128)(2,1)S(1)}, u32[]{:S(2)}, u32[]{:S(2)}) %collective-permute-start.16) | collective-permute-done | bytes 163872 | tf_op jit(solution)/shard_map/cond/branch_1_fun/ppermute | solution.py:33
  181.3 6.8 %collective-permute-done.15 = bf16[80,1024]{1,0:T(8,128)(2,1)S(1)} collective-permute-done((bf16[80,1024]{1,0:T(8,128)(2,1)S(1)}, bf16[80,1024]{1,0:T(8,128)(2,1)S(1)}, u32[]{:S(2)}, u32[]{:S(2)}) %collective-permute-start.15) | collective-permute-done | bytes 163872 | tf_op jit(solution)/shard_map/cond/branch_1_fun/ppermute | solution.py:33
  188.2 8.0 %collective-permute-done.14 = bf16[80,1024]{1,0:T(8,128)(2,1)S(1)} collective-permute-done((bf16[80,1024]{1,0:T(8,128)(2,1)S(1)}, bf16[80,1024]{1,0:T(8,128)(2,1)S(1)}, u32[]{:S(2)}, u32[]{:S(2)}) %collective-permute-start.14) | collective-permute-done | bytes 163872 | tf_op jit(solution)/shard_map/cond/branch_1_fun/ppermute | solution.py:33
  196.4 0.9 pad_maximum_fusion.1
  197.3 1.0 fusion.15
  198.3 14.2 %collective-permute-done.28.rest_2_ = bf16[320,1024]{1,0:T(8,128)(2,1)S(1)} collective-permute-done((bf16[320,1024]{1,0:T(8,128)(2,1)}, bf16[320,1024]{1,0:T(8,128)(2,1)S(1)}, u32[]{:S(2)}, u32[]{:S(2)}) %collective-permute-start.28) | collective-permute-done | bytes 655392 | tf_op jit(solution)/shard_map/ppermute | solution.py:33
  212.5 2.1 collective-permute-done.29.rest_3_
  214.6 0.8 copy-done.22
  215.4 8.9 %joined.1 = (f32[1024,2,1024]{2,1,0:T(2,128)}, f32[1024,1024]{1,0:T(8,128)}, f32[64,1024]{1,0:T(8,128)}, f32[16,1024]{1,0:T(8,128)}, f32[1,1024]{1,0:T(1,128)}, ...) custom-call(s32[1]{0:T(128)} %bitcast.21.place_ref, ...), custom_call_target="tpu_custom_call" | custom-call | flops 1 | bytes 1 | tf_op jit(solution)/shard_map/joined/pallas_call | solution.py:1055
  (121 shorter events, 4.5 us)
Async XLA Ops:
  7.2 207.4 %all-reduce.3.cloned.1.call-start = ((), (), s32[]{:S(2)}) async-start(), calls=%async_computation | async-start | bytes 8388608 | tf_op jit(solution)/shard_map/psum | solution.py:1208
  7.2 11.4 %collective-permute-start.18 = (bf16[256,512]{1,0:T(8,128)(2,1)}, bf16[256,512]{1,0:T(8,128)(2,1)S(1)}, u32[]{:S(2)}, u32[]{:S(2)}) collective-permute-start(bf16[256,512]{1,0:T(8,128)(2,1)} %own_ref.1), channel_id=1, source_target_pairs={{0,1},{1,0},{2,3},{3,2},{4,5},{5,4},{6,7},{7,6},{8,9},{9,8},{10,11... | collective-permute-start | bytes 786440 | tf_op jit(solution)/shard_map/ppermute | solution.py:33
  11.6 7.0 %collective-permute-start.20 = (bf16[16,512]{1,0:T(8,128)(2,1)}, bf16[16,512]{1,0:T(8,128)(2,1)S(1)}, u32[]{:S(2)}, u32[]{:S(2)}) collective-permute-start(bf16[16,512]{1,0:T(8,128)(2,1)} %edge_rows.1), channel_id=1, source_target_pairs={{0,3},{1,2},{2,5},{3,4},{4,7},{5,6},{6,9},{7,8},{8,11},{9,10},{10,... | collective-permute-start | bytes 49160 | tf_op jit(solution)/shard_map/ppermute | solution.py:51
  13.0 5.6 %collective-permute-start.19 = (bf16[16,512]{1,0:T(8,128)(2,1)}, bf16[16,512]{1,0:T(8,128)(2,1)S(1)}, u32[]{:S(2)}, u32[]{:S(2)}) collective-permute-start(bf16[16,512]{1,0:T(8,128)(2,1)} %edge_rows.1), channel_id=1, source_target_pairs={{0,2},{2,4},{4,6},{6,8},{8,10},{10,12},{12,14},{14,16},{16,18},{18... | collective-permute-start | bytes 49160 | tf_op jit(solution)/shard_map/ppermute | solution.py:28
  17.0 12.6 %collective-permute-start.22 = (bf16[256,512]{1,0:T(8,128)(2,1)}, bf16[256,512]{1,0:T(8,128)(2,1)S(1)}, u32[]{:S(2)}, u32[]{:S(2)}) collective-permute-start(bf16[256,512]{1,0:T(8,128)(2,1)} %param.27), channel_id=1, source_target_pairs={{0,1},{1,0},{2,3},{3,2},{4,5},{5,4},{6,7},{7,6},{8,9},{9,8},{10,11... | collective-permute-start | bytes 786440 | tf_op jit(solution)/shard_map/ppermute | solution.py:33
  18.6 0.7 copy-start.28
  21.6 4.0 %copy-start.18 = (bf16[96,1024]{1,0:T(8,128)(2,1)S(1)}, bf16[96,1024]{1,0:T(8,128)(2,1)}, u32[]{:S(2)}) copy-start(bf16[96,1024]{1,0:T(8,128)(2,1)} %select_ref.1) | copy-start | bytes 589828
  21.6 4.0 %copy-start.31 = (f32[4,1024]{1,0:T(4,128)S(1)}, f32[4,1024]{1,0:T(4,128)}, u32[]{:S(2)}) copy-start(f32[4,1024]{1,0:T(4,128)} %conv_weight_ref.1) | copy-start | bytes 49156
  21.6 8.1 %copy-start.14 = (bf16[256,512]{1,0:T(8,128)(2,1)S(1)}, bf16[256,512]{1,0:T(8,128)(2,1)}, u32[]{:S(2)}) copy-start(bf16[256,512]{1,0:T(8,128)(2,1)} %param.27) | copy-start | bytes 786436
  25.6 4.2 %copy-start = (bf16[1024,1024]{1,0:T(8,128)(2,1)S(1)}, bf16[1024,1024]{1,0:T(8,128)(2,1)}, u32[]{:S(2)}) copy-start(bf16[1024,1024]{1,0:T(8,128)(2,1)} %param.25) | copy-start | bytes 6291460
  28.7 4.6 %collective-permute-start.21 = (f32[96,256]{1,0:T(8,128)S(1)}, f32[96,256]{1,0:T(8,128)S(1)}, u32[]{:S(2)}, u32[]{:S(2)}) collective-permute-start(f32[96,256]{1,0:T(8,128)S(1)} %get-tuple-element.153.selected_ref), channel_id=1, source_target_pairs={{0,1},{1,0},{2,3},{3,2},{4,5},{5,4},{6,7},{7,6},{8,9},{9,8},{10,11... | collective-permute-start | bytes 294920 | tf_op jit(solution)/shard_map/ppermute | solution.py:33
  29.7 13.6 %copy-start.6 = (bf16[256,512]{1,0:T(8,128)(2,1)}, bf16[256,512]{1,0:T(8,128)(2,1)S(1)}, u32[]{:S(2)}) copy-start(bf16[256,512]{1,0:T(8,128)(2,1)S(1)} %get-tuple-element.232) | copy-start | bytes 786436
  29.7 13.6 %copy-start.7 = (bf16[256,512]{1,0:T(8,128)(2,1)}, bf16[256,512]{1,0:T(8,128)(2,1)S(1)}, u32[]{:S(2)}) copy-start(bf16[256,512]{1,0:T(8,128)(2,1)S(1)} %get-tuple-element.233) | copy-start | bytes 786436
  29.7 3.6 %copy-start.12 = (f32[16,1024]{1,0:T(8,128)S(1)}, f32[16,1024]{1,0:T(8,128)}, u32[]{:S(2)}) copy-start(f32[16,1024]{1,0:T(8,128)} %decay_log_ref.7) | copy-start | bytes 196612
  29.7 3.6 %copy-start.23 = (bf16[64,1024]{1,0:T(8,128)(2,1)S(1)}, bf16[64,1024]{1,0:T(8,128)(2,1)}, u32[]{:S(2)}) copy-start(bf16[64,1024]{1,0:T(8,128)(2,1)} %step_weight_ref.1) | copy-start | bytes 393220
  33.3 10.0 %copy-start.17 = (f32[96,256]{1,0:T(8,128)}, f32[96,256]{1,0:T(8,128)S(1)}, u32[]{:S(2)}) copy-start(f32[96,256]{1,0:T(8,128)S(1)} %collective-permute-done.21.other_ref) | copy-start | bytes 294916
  43.3 1.7 collective-permute-start.23
  46.8 5.2 %collective-permute-start.24 = (bf16[48,1024]{1,0:T(8,128)(2,1)}, bf16[48,1024]{1,0:T(8,128)(2,1)}, u32[]{:S(2)}, u32[]{:S(2)}) collective-permute-start(bf16[48,1024]{1,0:T(8,128)(2,1)} %get-tuple-element.158.own_ref), channel_id=1, source_target_pairs={{0,4},{2,6},{4,0},{6,2},{8,12},{10,14},{12,8},{14,10},{16,20},{18,... | collective-permute-start | bytes 294920 | tf_op jit(solution)/shard_map/ppermute | solution.py:33
  53.7 8.0 %collective-permute-start.25 = (bf16[16,1024]{1,0:T(8,128)(2,1)}, bf16[16,1024]{1,0:T(8,128)(2,1)S(1)}, u32[]{:S(2)}, u32[]{:S(2)}) collective-permute-start(bf16[16,1024]{1,0:T(8,128)(2,1)} %get-tuple-element.161), channel_id=1, source_target_pairs={{0,8},{2,10},{4,12},{6,14},{8,16},{10,18},{12,20},{14,22},{16,24},... | collective-permute-start | bytes 98312 | tf_op jit(solution)/shard_map/ppermute | solution.py:28
  58.3 15.3 %collective-permute-start.26 = (bf16[16,1024]{1,0:T(8,128)(2,1)}, bf16[16,1024]{1,0:T(8,128)(2,1)S(1)}, u32[]{:S(2)}, u32[]{:S(2)}) collective-permute-start(bf16[16,1024]{1,0:T(8,128)(2,1)} %get-tuple-element.164), channel_id=1, source_target_pairs={{8,0},{10,2},{12,4},{14,6},{16,8},{18,10},{20,12},{22,14},{24,16},... | collective-permute-start | bytes 98312 | tf_op jit(solution)/shard_map/ppermute | solution.py:28
  97.2 5.0 %copy-start.16 = (f32[256,1024]{1,0:T(8,128)S(1)}, f32[256,1024]{1,0:T(8,128)}, u32[]{:S(2)}) copy-start(f32[256,1024]{1,0:T(8,128)} %get-tuple-element.79.convolved_ref) | copy-start | bytes 3145732 | tf_op jit(solution)/shard_map/cond
  97.2 5.0 %copy-start.19 = (bf16[96,1024]{1,0:T(8,128)(2,1)S(1)}, bf16[96,1024]{1,0:T(8,128)(2,1)}, u32[]{:S(2)}) copy-start(bf16[96,1024]{1,0:T(8,128)(2,1)} %get-tuple-element.77.select_ref) | copy-start | bytes 589828 | tf_op jit(solution)/shard_map/cond
  97.2 5.0 %collective-permute-start = (f32[96,256]{1,0:T(8,128)}, f32[96,256]{1,0:T(8,128)}, u32[]{:S(2)}, u32[]{:S(2)}) collective-permute-start(f32[96,256]{1,0:T(8,128)} %get-tuple-element.76.select_grad_ref.refs_1_), channel_id=1, source_target_pairs={{0,1},{1,0},{2,3},{3,2},{4,5},{5,4},{6,7},{7,6},{8,9},{9,8},{10,11... | collective-permute-start | bytes 294920 | tf_op jit(solution)/shard_map/cond/branch_1_fun/ppermute | solution.py:33
  99.5 10.1 %collective-permute-start.4 = (bf16[256,256]{1,0:T(8,128)(2,1)}, bf16[256,256]{1,0:T(8,128)(2,1)S(1)}, u32[]{:S(2)}, u32[]{:S(2)}) collective-permute-start(bf16[256,256]{1,0:T(8,128)(2,1)} %get-tuple-element.221), channel_id=1, source_target_pairs={{0,6},{2,4},{4,2},{6,0},{8,14},{10,12},{12,10},{14,8},{16,22},{18,... | collective-permute-start | bytes 393224 | tf_op jit(solution)/shard_map/cond/branch_1_fun/ppermute | solution.py:33
  99.5 10.1 %collective-permute-start.3 = (bf16[256,256]{1,0:T(8,128)(2,1)}, bf16[256,256]{1,0:T(8,128)(2,1)S(1)}, u32[]{:S(2)}, u32[]{:S(2)}) collective-permute-start(bf16[256,256]{1,0:T(8,128)(2,1)} %get-tuple-element.222), channel_id=1, source_target_pairs={{0,2},{2,0},{4,6},{6,4},{8,10},{10,8},{12,14},{14,12},{16,18},{18,... | collective-permute-start | bytes 393224 | tf_op jit(solution)/shard_map/cond/branch_1_fun/ppermute | solution.py:33
  100.2 9.4 %collective-permute-start.2 = (bf16[256,256]{1,0:T(8,128)(2,1)}, bf16[256,256]{1,0:T(8,128)(2,1)S(1)}, u32[]{:S(2)}, u32[]{:S(2)}) collective-permute-start(bf16[256,256]{1,0:T(8,128)(2,1)} %get-tuple-element.223), channel_id=1, source_target_pairs={{0,4},{2,6},{4,0},{6,2},{8,12},{10,14},{12,8},{14,10},{16,20},{18,... | collective-permute-start | bytes 393224 | tf_op jit(solution)/shard_map/cond/branch_1_fun/ppermute | solution.py:33
  102.2 5.7 %copy-start.30 = (f32[256,1]{1,0:T(8,128)S(1)}, f32[256,1]{1,0:T(8,128)}, u32[]{:S(2)}) copy-start(f32[256,1]{1,0:T(8,128)} %get-tuple-element.208) | copy-start | bytes 3076 | tf_op jit(solution)/shard_map/cond
  106.2 12.4 %copy-start.35 = (f32[1024]{0:T(1024)S(1)}, f32[1024]{0:T(1024)}, u32[]{:S(2)}) copy-start(f32[1024]{0:T(1024)} %get-tuple-element.89) | copy-start | bytes 12292 | tf_op jit(solution)/shard_map/cond
  106.2 12.4 %copy-start.38 = (bf16[256,1024]{1,0:T(8,128)(2,1)S(1)}, bf16[256,1024]{1,0:T(8,128)(2,1)}, u32[]{:S(2)}) copy-start(bf16[256,1024]{1,0:T(8,128)(2,1)} %get-tuple-element.87) | copy-start | bytes 1572868 | tf_op jit(solution)/shard_map/cond
  106.2 3.4 %collective-permute-start.1 = (f32[8,1024]{1,0:T(8,128)}, f32[8,1024]{1,0:T(8,128)S(1)}, u32[]{:S(2)}, u32[]{:S(2)}) collective-permute-start(f32[8,1024]{1,0:T(8,128)} %get-tuple-element.83), channel_id=1, source_target_pairs={{2,0},{4,2},{6,4},{8,6},{10,8},{12,10},{14,12},{16,14},{18,16},{20... | collective-permute-start | bytes 98312 | tf_op jit(solution)/shard_map/cond/branch_1_fun/ppermute | solution.py:28
  109.7 0.7 copy-start.26
  109.7 0.7 copy-start.27
  111.9 25.8 %collective-permute-start.5 = (bf16[256,1024]{1,0:T(8,128)(2,1)}, bf16[256,1024]{1,0:T(8,128)(2,1)S(1)}, u32[]{:S(2)}, u32[]{:S(2)}) collective-permute-start(bf16[256,1024]{1,0:T(8,128)(2,1)} %patched.1.wait_ref.own_ref), channel_id=1, source_target_pairs={{0,4},{2,6},{4,0},{6,2},{8,12},{10,14},{12,8},{14,10},{16,20},{18,... | collective-permute-start | bytes 1572872 | tf_op jit(solution)/shard_map/cond/branch_1_fun/ppermute | solution.py:33
  115.4 9.7 %collective-permute-start.7 = (bf16[128,1024]{1,0:T(8,128)(2,1)}, bf16[128,1024]{1,0:T(8,128)(2,1)S(1)}, u32[]{:S(2)}, u32[]{:S(2)}) collective-permute-start(bf16[128,1024]{1,0:T(8,128)(2,1)} %get-tuple-element.93), channel_id=1, source_target_pairs={{0,2},{2,0},{4,6},{6,4},{8,10},{10,8},{12,14},{14,12},{16,18},{18,... | collective-permute-start | bytes 786440 | tf_op jit(solution)/shard_map/cond/branch_1_fun/ppermute | solution.py:33
  122.9 18.5 %copy-start.4 = (f32[256,1024]{1,0:T(8,128)}, f32[256,1024]{1,0:T(8,128)S(1)}, u32[]{:S(2)}) copy-start(f32[256,1024]{1,0:T(8,128)S(1)} %get-tuple-element.231) | copy-start | bytes 3145732 | tf_op jit(solution)/shard_map/cond
  122.9 16.4 %copy-start.2 = (bf16[256,1024]{1,0:T(8,128)(2,1)S(1)}, bf16[256,1024]{1,0:T(8,128)(2,1)}, u32[]{:S(2)}) copy-start(bf16[256,1024]{1,0:T(8,128)(2,1)} %patched.1.wait_ref.own_ref) | copy-start | bytes 1572868 | tf_op jit(solution)/shard_map/cond
  123.0 14.6 %collective-permute-start.9 = (f32[256,512]{1,0:T(8,128)S(1)}, f32[256,512]{1,0:T(8,128)S(1)}, u32[]{:S(2)}, u32[]{:S(2)}) collective-permute-start(f32[256,512]{1,0:T(8,128)S(1)} %slice_select_fusion.1), channel_id=1, source_target_pairs={{0,1},{1,0},{2,3},{3,2},{4,5},{5,4},{6,7},{7,6},{8,9},{9,8},{10,11... | collective-permute-start | bytes 1572872 | tf_op jit(solution)/shard_map/cond/branch_1_fun/ppermute | solution.py:33
  124.5 12.6 %collective-permute-start.6 = (f32[1,1280]{1,0:T(1,128)S(1)}, f32[1,1280]{1,0:T(1,128)S(1)}, u32[]{:S(2)}, u32[]{:S(2)}) collective-permute-start(f32[1,1280]{1,0:T(1,128)S(1)} %pad_maximum_fusion.5), channel_id=1, source_target_pairs={{0,1},{1,0},{2,3},{3,2},{4,5},{5,4},{6,7},{7,6},{8,9},{9,8},{10,11... | collective-permute-start | bytes 15368 | tf_op jit(solution)/shard_map/cond/branch_1_fun/ppermute | solution.py:33
  125.1 0.7 copy-start.29
  127.7 9.9 %collective-permute-start.8 = (bf16[64,1024]{1,0:T(8,128)(2,1)}, bf16[64,1024]{1,0:T(8,128)(2,1)S(1)}, u32[]{:S(2)}, u32[]{:S(2)}) collective-permute-start(bf16[64,1024]{1,0:T(8,128)(2,1)} %get-tuple-element.94), channel_id=1, source_target_pairs={{0,4},{2,6},{4,0},{6,2},{8,12},{10,14},{12,8},{14,10},{16,20},{18,... | collective-permute-start | bytes 393224 | tf_op jit(solution)/shard_map/cond/branch_1_fun/ppermute | solution.py:33
  137.7 3.8 %copy-start.32 = (f32[1,1280]{1,0:T(1,128)S(1)}, f32[1,1280]{1,0:T(1,128)}, u32[]{:S(2)}) copy-start(f32[1,1280]{1,0:T(1,128)} %fusion.21.refs_1_) | copy-start | bytes 15364 | tf_op jit(solution)/shard_map/cond
  137.7 0.8 copy-start.10
  138.5 0.8 copy-start.3
  139.3 13.1 %copy-start.9 = (bf16[256,1024]{1,0:T(8,128)(2,1)S(1)}, bf16[256,1024]{1,0:T(8,128)(2,1)}, u32[]{:S(2)}) copy-start(bf16[256,1024]{1,0:T(8,128)(2,1)} %get-tuple-element.102.refs_0_) | copy-start | bytes 1572868 | tf_op jit(solution)/shard_map/cond
  141.5 3.0 %collective-permute-start.10 = (bf16[512,1024]{1,0:T(8,128)(2,1)}, bf16[512,1024]{1,0:T(8,128)(2,1)}, u32[]{:S(2)}, u32[]{:S(2)}) collective-permute-start(bf16[512,1024]{1,0:T(8,128)(2,1)} %pad_maximum_fusion), channel_id=1, source_target_pairs={{0,2},{2,0},{4,6},{6,4},{8,10},{10,8},{12,14},{14,12},{16,18},{18,... | collective-permute-start | bytes 3145736 | tf_op jit(solution)/shard_map/cond/branch_1_fun/ppermute | solution.py:33
  144.5 8.0 %copy-start.1 = (bf16[1024,1024]{1,0:T(8,128)(2,1)S(1)}, bf16[1024,1024]{1,0:T(8,128)(2,1)}, u32[]{:S(2)}) copy-start(bf16[1024,1024]{1,0:T(8,128)(2,1)} %get-tuple-element.103) | copy-start | bytes 6291460 | tf_op jit(solution)/shard_map/cond
  148.0 10.9 %collective-permute-start.11 = (bf16[80,1024]{1,0:T(8,128)(2,1)}, bf16[80,1024]{1,0:T(8,128)(2,1)S(1)}, u32[]{:S(2)}, u32[]{:S(2)}) collective-permute-start(bf16[80,1024]{1,0:T(8,128)(2,1)} %get-tuple-element.98), channel_id=1, source_target_pairs={{0,8},{2,10},{4,12},{6,14},{8,0},{10,2},{12,4},{14,6},{16,24},{18,... | collective-permute-start | bytes 491528 | tf_op jit(solution)/shard_map/cond/branch_1_fun/ppermute | solution.py:33
  149.6 15.4 %collective-permute-start.12 = (bf16[80,1024]{1,0:T(8,128)(2,1)}, bf16[80,1024]{1,0:T(8,128)(2,1)S(1)}, u32[]{:S(2)}, u32[]{:S(2)}) collective-permute-start(bf16[80,1024]{1,0:T(8,128)(2,1)} %get-tuple-element.99), channel_id=1, source_target_pairs={{0,16},{2,18},{4,20},{6,22},{8,24},{10,26},{12,28},{14,30},{16,0},... | collective-permute-start | bytes 491528 | tf_op jit(solution)/shard_map/cond/branch_1_fun/ppermute | solution.py:33
  150.7 14.3 %collective-permute-start.13 = (bf16[80,1024]{1,0:T(8,128)(2,1)}, bf16[80,1024]{1,0:T(8,128)(2,1)S(1)}, u32[]{:S(2)}, u32[]{:S(2)}) collective-permute-start(bf16[80,1024]{1,0:T(8,128)(2,1)} %get-tuple-element.100), channel_id=1, source_target_pairs={{0,24},{2,26},{4,28},{6,30},{8,16},{10,18},{12,20},{14,22},{16,8},... | collective-permute-start | bytes 491528 | tf_op jit(solution)/shard_map/cond/branch_1_fun/ppermute | solution.py:33
  152.4 12.6 %copy-start.13 = (f32[80,1024]{1,0:T(8,128)S(1)}, f32[80,1024]{1,0:T(8,128)}, u32[]{:S(2)}) copy-start(f32[80,1024]{1,0:T(8,128)} %get-tuple-element.97.refs_1_) | copy-start | bytes 983044 | tf_op jit(solution)/shard_map/cond
  165.1 16.2 %collective-permute-start.16 = (bf16[80,1024]{1,0:T(8,128)(2,1)S(1)}, bf16[80,1024]{1,0:T(8,128)(2,1)S(1)}, u32[]{:S(2)}, u32[]{:S(2)}) collective-permute-start(bf16[80,1024]{1,0:T(8,128)(2,1)S(1)} %pad_maximum_fusion.4), channel_id=1, source_target_pairs={{0,8},{2,10},{4,12},{6,14},{8,0},{10,2},{12,4},{14,6},{16,24},{18,... | collective-permute-start | bytes 491528 | tf_op jit(solution)/shard_map/cond/branch_1_fun/ppermute | solution.py:33
  171.7 25.5 %copy-start.5 = (f32[256,1024]{1,0:T(8,128)S(1)}, f32[256,1024]{1,0:T(8,128)}, u32[]{:S(2)}) copy-start(f32[256,1024]{1,0:T(8,128)} %copy-done.4) | copy-start | bytes 3145732 | tf_op jit(solution)/shard_map/cond
  171.7 25.5 %copy-start.8 = (bf16[256,512]{1,0:T(8,128)(2,1)S(1)}, bf16[256,512]{1,0:T(8,128)(2,1)}, u32[]{:S(2)}) copy-start(bf16[256,512]{1,0:T(8,128)(2,1)} %get-tuple-element.101) | copy-start | bytes 786436 | tf_op jit(solution)/shard_map/cond
  171.7 25.5 %copy-start.11 = (f32[256,512]{1,0:T(8,128)S(1)}, f32[256,512]{1,0:T(8,128)}, u32[]{:S(2)}) copy-start(f32[256,512]{1,0:T(8,128)} %copy-done.10) | copy-start | bytes 1572868 | tf_op jit(solution)/shard_map/cond
  171.8 25.5 %copy-start.15 = (bf16[256,512]{1,0:T(8,128)(2,1)S(1)}, bf16[256,512]{1,0:T(8,128)(2,1)}, u32[]{:S(2)}) copy-start(bf16[256,512]{1,0:T(8,128)(2,1)} %get-tuple-element.104) | copy-start | bytes 786436 | tf_op jit(solution)/shard_map/cond
  171.8 25.5 %collective-permute-start.17 = (f32[256,512]{1,0:T(8,128)S(1)}, f32[256,512]{1,0:T(8,128)S(1)}, u32[]{:S(2)}, u32[]{:S(2)}) collective-permute-start(f32[256,512]{1,0:T(8,128)S(1)} %slice_select_fusion), channel_id=1, source_target_pairs={{0,1},{1,0},{2,3},{3,2},{4,5},{5,4},{6,7},{7,6},{8,9},{9,8},{10,11... | collective-permute-start | bytes 1572872 | tf_op jit(solution)/shard_map/cond/branch_1_fun/ppermute | solution.py:33
  173.3 14.9 %collective-permute-start.15 = (bf16[80,1024]{1,0:T(8,128)(2,1)S(1)}, bf16[80,1024]{1,0:T(8,128)(2,1)S(1)}, u32[]{:S(2)}, u32[]{:S(2)}) collective-permute-start(bf16[80,1024]{1,0:T(8,128)(2,1)S(1)} %pad_maximum_fusion.4), channel_id=1, source_target_pairs={{0,16},{2,18},{4,20},{6,22},{8,24},{10,26},{12,28},{14,30},{16,0},... | collective-permute-start | bytes 491528 | tf_op jit(solution)/shard_map/cond/branch_1_fun/ppermute | solution.py:33
  175.1 21.1 %collective-permute-start.14 = (bf16[80,1024]{1,0:T(8,128)(2,1)S(1)}, bf16[80,1024]{1,0:T(8,128)(2,1)S(1)}, u32[]{:S(2)}, u32[]{:S(2)}) collective-permute-start(bf16[80,1024]{1,0:T(8,128)(2,1)S(1)} %pad_maximum_fusion.4), channel_id=1, source_target_pairs={{0,24},{2,26},{4,28},{6,30},{8,16},{10,18},{12,20},{14,22},{16,8},... | collective-permute-start | bytes 491528 | tf_op jit(solution)/shard_map/cond/branch_1_fun/ppermute | solution.py:33
  198.3 14.2 %collective-permute-start.28 = (bf16[320,1024]{1,0:T(8,128)(2,1)}, bf16[320,1024]{1,0:T(8,128)(2,1)S(1)}, u32[]{:S(2)}, u32[]{:S(2)}) collective-permute-start(bf16[320,1024]{1,0:T(8,128)(2,1)} %get-tuple-element.174.rest_0_), channel_id=1, source_target_pairs={{0,4},{2,6},{4,0},{6,2},{8,12},{10,14},{12,8},{14,10},{16,20},{18,... | collective-permute-start | bytes 1966088 | tf_op jit(solution)/shard_map/ppermute | solution.py:33
  198.3 14.2 %collective-permute-start.27 = (bf16[320,1024]{1,0:T(8,128)(2,1)}, bf16[320,1024]{1,0:T(8,128)(2,1)S(1)}, u32[]{:S(2)}, u32[]{:S(2)}) collective-permute-start(bf16[320,1024]{1,0:T(8,128)(2,1)} %get-tuple-element.174.rest_0_), channel_id=1, source_target_pairs={{0,2},{2,0},{4,6},{6,4},{8,10},{10,8},{12,14},{14,12},{16,18},{18,... | collective-permute-start | bytes 1966088 | tf_op jit(solution)/shard_map/ppermute | solution.py:33
  212.5 2.1 copy-start.20
  212.5 2.1 collective-permute-start.29
  212.5 2.1 copy-start.21
  214.6 0.8 copy-start.22
  (6 other events, 3.7 us)
Sparse Core Ops, SparseCore 0:
  73.8 134.5 all-reduce.2

commit v23 on v22

--- a/solution.py
+++ b/solution.py
@@ -60,7 +60,7 @@
     while bit < lax.axis_size("wide"):
         bits.append(bit)
         bit *= 2
-    return [tuple(bits[k : k + size]) for k in range(0, len(bits), size)]
+    return [tuple(bits[k : k + size][::-1]) for k in range(0, len(bits), size)]
 
 
 def flips(bits):
@@ -1256,17 +1256,14 @@
         gain_part = jnp.sum(normed_part * whole * inverse, axis=0, keepdims=True)
         row_part = jnp.sum(normed_part * norm_gain * whole, axis=1)[None]
         first_bits, *more_bits = group_bits(2)
-        narrow_sums = jnp.concatenate([gain_part, row_part], axis=1)
-        narrow_sums = narrow_sums + swapped(narrow_sums, "narrow", 1)
-        gain_sum = narrow_sums[:, : 2 * features]
+        gain_sum = gain_part + swapped(gain_part, "narrow", 1)
         for bit in (bit for bits in more_bits for bit in bits):
             gain_sum = gain_sum + swapped(gain_sum, "wide", bit)
-        normed_mine, normed_other = narrow_halves(normed_part)
-        normed_theirs = swapped(normed_other, "narrow", 1)
-        near = after(near, narrow_sums, smalls[1], normed_theirs)
+        row_theirs = swapped(row_part, "narrow", 1)
+        near = after(near, gain_sum, row_theirs, smalls[1])
         far = swapped(jnp.concatenate([inner_grad, near]), "wide", 1)
         keep, *sends = inner_quarter(
-            (wide_place >> 2 & 3)[None],
+            ((wide_place >> 3 & 1) + 2 * (wide_place >> 2 & 1))[None],
             inner_grad,
             near,
             far,
@@ -1274,11 +1271,13 @@
             smalls,
             [],
         )
+        normed_mine, normed_other = narrow_halves(normed_part)
+        normed_theirs = swapped(after(normed_other, keep), "narrow", 1)
         out_part = jnp.dot(after(gated, keep), out_weight, preferred_element_type=f32)
         out_mine, out_other = narrow_halves(out_part)
         out_theirs = swapped(out_other, "narrow", 1)
         layer_out = (tokens.astype(f32) + (out_mine + out_theirs)).astype(bf16)
-        row_sum = narrow_sums[:, 2 * features :].reshape(rows, 1)
+        row_sum = (row_part + row_theirs).reshape(rows, 1)
         gain_mine = jnp.where(right_half, norm_gain[features:], norm_gain[:features])
         whole_grad = inverse * (gain_mine * (normed_mine + normed_theirs)) - tokens.astype(f32) * (
             inverse * inverse * inverse
@@ -1294,7 +1293,8 @@
             held = gathered(held, bits)
         spare = jnp.broadcast_to(gain_sum, (block_rows - used_rows, gain_sum.shape[1]))
         held = jnp.concatenate([held[: held.shape[0] - spare.shape[0]], spare.astype(bf16)])
-        held = gathered(held, first_bits)
+        for bit in first_bits:
+            held = gathered(held, (bit,))
         return held, layer_out, tokens_grad
 
     kinds = jax.eval_shape(after_forward, products)

time: 232 us -> 233 us (level)
  starting transfers between devices: 46.5 us -> 43.6 us
  waiting for transfers between devices: 69.9 us -> 72.4 us
    ppermute x25, starting transfers between devices: 33.4 us -> 30.6 us  [swapped(): return lax.ppermute(array, axis, [(i, i ^ bit) for i in range(peers)])]
    ppermute x25, waiting for transfers between devices: 68.1 us -> 70.7 us  [swapped(): return lax.ppermute(array, axis, [(i, i ^ bit) for i in range(peers)])]
  transfers between devices with their start and end apart: 31 -> 31, of which waited for: 14 -> 15; matrix products, arithmetic and copies ran while one was open for 8% -> 8% of each run, Pallas kernels for 24% -> 24%
where the time goes in v23:
time: 233 us; the launch traced here: 232 us
  Pallas kernels  77 us (33%)
  waiting for transfers between devices  72.4 us (31%)
  starting transfers between devices  43.6 us (19%)
  between operations  14.3 us (6%)
  matrix products  10.8 us (5%)
  other arithmetic  6.99 us (3%)
  local copies, waits for them, and re-layouts  6.5 us (3%)
    ppermute x25, waiting for transfers between devices, swapped(): return lax.ppermute(array, axis, [(i, i ^ bit) for i in range(peers)])  70.7 us
    pallas_call x5, Pallas kernels, call(): pl.pallas_call(kernel, grid=(width // scan_width,), in_specs=in_specs, ou...  51.9 us
    ppermute x25, starting transfers between devices, swapped(): return lax.ppermute(array, axis, [(i, i ^ bit) for i in range(peers)])  30.6 us
    ppermute x4, starting transfers between devices, passed_along(): return lax.ppermute(array, axis, pairs)  11.7 us
    pallas_call x1, Pallas kernels, joined(): pl.pallas_call(functools.partial(join_kernel, small_rows=small_rows), gri...  8.91 us
  transfers between devices with their start and end apart: 31, of which 15 were waited for; matrix products, arithmetic and copies ran while one was open for 8% of the time, Pallas kernels for 24%

profile of v23, /device:TPU:0, one launch (start us, length us, event | category | flops | bytes accessed | tf_op | source)
XLA Modules:
  0.0 231.9 jit_solution(18123398832511466745)
XLA Ops:
  7.2 3.0 %collective-permute-start.18 = (bf16[256,512]{1,0:T(8,128)(2,1)}, bf16[256,512]{1,0:T(8,128)(2,1)S(1)}, u32[]{:S(2)}, u32[]{:S(2)}) collective-permute-start(bf16[256,512]{1,0:T(8,128)(2,1)} %own_ref.1), channel_id=1, source_target_pairs={{0,1},{1,0},{2,3},{3,2},{4,5},{5,4},{6,7},{7,6},{8,9},{9,8},{10,11... | collective-permute-start | bytes 786440 | tf_op jit(solution)/shard_map/ppermute | solution.py:33
  10.3 1.4 edge_rows.1
  11.6 1.3 collective-permute-start.20
  13.0 4.0 %collective-permute-start.19 = (bf16[16,512]{1,0:T(8,128)(2,1)}, bf16[16,512]{1,0:T(8,128)(2,1)S(1)}, u32[]{:S(2)}, u32[]{:S(2)}) collective-permute-start(bf16[16,512]{1,0:T(8,128)(2,1)} %edge_rows.1), channel_id=1, source_target_pairs={{0,2},{2,4},{4,6},{6,8},{8,10},{10,12},{12,14},{14,16},{16,18},{18... | collective-permute-start | bytes 49160 | tf_op jit(solution)/shard_map/ppermute | solution.py:28
  17.0 1.6 collective-permute-start.22
  19.3 2.3 normalized.1
  21.6 4.0 %fusion.25.inner_ref.gate_ref = bf16[2,272,1024]{2,1,0:T(8,128)(2,1)S(1)} fusion(bf16[1024,2,1024]{2,1,0:T(2,128)(2,1)} %param.17, bf16[272,1024]{1,0:T(8,128)(2,1)} %get-tuple-element.151), kind=kOutput, calls=%fused_computation.44 | convolution fusion | flops 1141407744 | bytes 5865472 | tf_op jit(solution)/shard_map/td,dce->cte/dot_general | solution.py:1169
  25.6 3.1 %convolve.1 = (f32[256,1024]{1,0:T(8,128)}, bf16[256,1024]{1,0:T(8,128)(2,1)S(1)}, f32[96,256]{1,0:T(8,128)S(1)}) custom-call(bf16[2,272,1024]{2,1,0:T(8,128)(2,1)S(1)} %fusion.25.inner_ref.gate_ref, f32[4,1024]{1,0:T(4,128)S(1)} %copy-done.28, f32[1,1024]{1,0:T(1,128)} %bitcast.40, bf16[96,1024]{1,0:T(8,128)(2,1)S(1)} %copy-done.15, ...), custom_call_target="tpu_custom_call" | custom-call | flops 1 | bytes 1 | tf_op jit(solution)/shard_map/convolve/pallas_call | solution.py:127
  28.7 0.9 collective-permute-start.21
  29.8 0.7 fusion.29.gated_grad_ref
  30.5 2.8 %collective-permute-done.21.other_ref = f32[96,256]{1,0:T(8,128)S(1)} collective-permute-done((f32[96,256]{1,0:T(8,128)S(1)}, f32[96,256]{1,0:T(8,128)S(1)}, u32[]{:S(2)}, u32[]{:S(2)}) %collective-permute-start.21) | collective-permute-done | bytes 98336 | tf_op jit(solution)/shard_map/ppermute | solution.py:33
  33.4 10.0 %scan_ends.1 = (f32[256,1024]{1,0:T(8,128)}, f32[256,1024]{1,0:T(8,128)}, bf16[48,1024]{1,0:T(8,128)(2,1)}) custom-call(f32[96,256]{1,0:T(8,128)S(1)} %get-tuple-element.153.selected_ref, f32[96,256]{1,0:T(8,128)S(1)} %collective-permute-done.21.other_ref, bf16[64,1024]{1,0:T(8,128)(2,1)S(1)} %copy-done.20, f32[1,1024]{1,0:T(1,128)} %bitcast.41, ...), custom_call_target="tpu_custom_call" | custom-call | flops 1 | bytes 1 | tf_op jit(solution)/shard_map/scan_ends/pallas_call | solution.py:127
  43.4 1.6 collective-permute-done.23.other_ref
  45.1 1.7 carry_round.2
  46.8 1.7 collective-permute-start.24
  48.5 3.5 %collective-permute-done.24.other_ref = bf16[48,1024]{1,0:T(8,128)(2,1)} collective-permute-done((bf16[48,1024]{1,0:T(8,128)(2,1)}, bf16[48,1024]{1,0:T(8,128)(2,1)}, u32[]{:S(2)}, u32[]{:S(2)}) %collective-permute-start.24) | collective-permute-done | bytes 98336 | tf_op jit(solution)/shard_map/ppermute | solution.py:33
  51.9 1.8 carry_round.3
  53.7 4.6 %collective-permute-start.25 = (bf16[16,1024]{1,0:T(8,128)(2,1)}, bf16[16,1024]{1,0:T(8,128)(2,1)S(1)}, u32[]{:S(2)}, u32[]{:S(2)}) collective-permute-start(bf16[16,1024]{1,0:T(8,128)(2,1)} %get-tuple-element.161), channel_id=1, source_target_pairs={{0,8},{2,10},{4,12},{6,14},{8,16},{10,18},{12,20},{14,22},{16,24},... | collective-permute-start | bytes 98312 | tf_op jit(solution)/shard_map/ppermute | solution.py:28
  58.3 1.5 collective-permute-start.26
  59.8 1.9 pad_maximum_fusion.4.cot_ref
  61.7 0.6 copy-done.29
  62.3 11.3 %scan_forward.1 = (bf16[256,1024]{1,0:T(8,128)(2,1)}, bf16[256,1024]{1,0:T(8,128)(2,1)}, bf16[1024,1024]{1,0:T(8,128)(2,1)}, bf16[1024,1024]{1,0:T(8,128)(2,1)}, f32[16,1024]{1,0:T(8,128)}) custom-call(f32[96,256]{1,0:T(8,128)S(1)} %get-tuple-element.153.selected_ref, f32[96,256]{1,0:T(8,128)} %copy-done.14, f32[256,1024]{1,0:T(8,128)} %get-tuple-element.156.step_ref, ...), custom_call_target="tpu_custom_call" | custom-call | flops 1 | bytes 1 | tf_op jit(solution)/shard_map/scan_forward/pallas_call | solution.py:127
  73.6 123.3 %conditional.1 = (bf16[320,1024]{1,0:T(8,128)(2,1)}, bf16[256,512]{1,0:T(8,128)(2,1)}, bf16[256,512]{1,0:T(8,128)(2,1)}) conditional(s32[]{:T(128)} %convert_element_type.43, () %tuple.16, (s32[]{:T(128)}, f32[1024]{0:T(1024)}, f32[96,256]{1,0:T(8,128)S(1)}, f32[96,256]{1,0:T(8,128)}, f32[256,1024]{1,0:T(8,128)}, /*index=5*/f32[256,1024]{1,0:T(8,128)}, ...), branch_computations={%region_0.1_spmd, %region_1.4_spmd} | conditional | flops 1621612800 | bytes 77649664 | solution.py:1301
  73.6 23.5 %scan_backward.1 = (f32[256,1024]{1,0:T(8,128)}, f32[96,256]{1,0:T(8,128)}, f32[82,1024]{1,0:T(8,128)}) custom-call(f32[96,256]{1,0:T(8,128)S(1)} %get-tuple-element.62.selected_ref, f32[96,256]{1,0:T(8,128)} %get-tuple-element.63.other_ref, f32[256,1024]{1,0:T(8,128)} %get-tuple-element.64.step_pre_ref, f32[256,1024]{1,0:T(8,128)} %get-tuple-element.65.step_ref, ...), custom_call_target="tpu_custom_call" | custom-call | flops 1 | bytes 1 | tf_op jit(solution)/shard_map/cond/branch_1_fun/scan_backward/pallas_call | solution.py:127
  97.2 1.5 collective-permute-start
  98.7 0.8 constant_dynamic-slice_fusion
  99.5 0.7 collective-permute-start.3
  100.2 1.4 collective-permute-start.2
  102.2 4.0 %convolve_grad.1 = (bf16[256,1024]{1,0:T(8,128)(2,1)}, f32[8,1024]{1,0:T(8,128)}, f32[8,1024]{1,0:T(8,128)}, f32[101,1024]{1,0:T(8,128)}) custom-call(f32[96,256]{1,0:T(8,128)} %get-tuple-element.76.select_grad_ref.refs_1_, f32[96,256]{1,0:T(8,128)} %collective-permute-done.other_ref, bf16[96,1024]{1,0:T(8,128)(2,1)S(1)} %copy-done.16, ...), custom_call_target="tpu_custom_call" | custom-call | flops 1 | bytes 1 | tf_op jit(solution)/shard_map/cond/branch_1_fun/convolve_grad/pallas_call | solution.py:127
  106.2 1.6 collective-permute-start.1
  108.0 1.7 collective-permute-done.1.next_ref
  110.4 1.5 patched.1.wait_ref.own_ref
  111.9 1.4 collective-permute-start.5
  113.2 2.2 small_halves.1
  115.5 3.1 %collective-permute-start.8 = (bf16[128,1024]{1,0:T(8,128)(2,1)}, bf16[128,1024]{1,0:T(8,128)(2,1)S(1)}, u32[]{:S(2)}, u32[]{:S(2)}) collective-permute-start(bf16[128,1024]{1,0:T(8,128)(2,1)} %get-tuple-element.93), channel_id=1, source_target_pairs={{0,2},{2,0},{4,6},{6,4},{8,10},{10,8},{12,14},{14,12},{16,18},{18,... | collective-permute-start | bytes 786440 | tf_op jit(solution)/shard_map/cond/branch_1_fun/ppermute | solution.py:33
  118.6 4.4 %fusion.7 = (f32[256]{0:T(256)S(1)}, f32[1024]{0:T(1024)S(1)}, f32[256,1024]{1,0:T(8,128)S(1)}) fusion(bf16[256,1024]{1,0:T(8,128)(2,1)S(1)} %copy-done.36, f32[1024]{0:T(1024)S(1)} %copy-done.31, f32[256]{0:T(256)S(1)} %bitcast.38, bf16[1024,2,1024]{2,1,0:T(2,128)(2,1)} %get-tuple-element.206, bf16[1,256,1024]{2,1,0:T(8,128)(2,1)} %bitcast.48, ...), kind=kOutput, calls=%fused_computation.7 | convolution fusion | flops 1076099840 | bytes 6825984 | tf_op jit(solution)/shard_map/cond/branch_1_fun/cte,dce->td/dot_general | solution.py:1253
  123.0 1.5 collective-permute-start.6
  124.4 0.6 collective-permute-start.7
  125.1 0.7 copy-done.26
  125.8 1.9 folded.1
  128.4 5.1 %collective-permute-done.9.refs_3_.arrived_ref = bf16[64,1024]{1,0:T(8,128)(2,1)S(1)} collective-permute-done((bf16[64,1024]{1,0:T(8,128)(2,1)}, bf16[64,1024]{1,0:T(8,128)(2,1)S(1)}, u32[]{:S(2)}, u32[]{:S(2)}) %collective-permute-start.9) | collective-permute-done | bytes 131104 | tf_op jit(solution)/shard_map/cond/branch_1_fun/ppermute | solution.py:33
  133.6 0.6 copy-done.24
  134.4 1.1 pad_maximum_fusion
  135.7 0.9 slice_select_fusion.refs_0_
  136.5 1.7 collective-permute-done.10.far_ref
  138.3 1.0 copy-done.10
  139.3 3.5 %inner_quarter.1 = (f32[80,1024]{1,0:T(8,128)}, bf16[80,1024]{1,0:T(8,128)(2,1)}, bf16[80,1024]{1,0:T(8,128)(2,1)}, bf16[80,1024]{1,0:T(8,128)(2,1)}) custom-call(s32[1]{0:T(128)} %bitcast.place_ref, bf16[256,1024]{1,0:T(8,128)(2,1)} %patched.1.wait_ref.own_ref, bf16[256,1024]{1,0:T(8,128)(2,1)} %after.6.near_ref, bf16[512,1024]{1,0:T(8,128)(2,1)} %copy-done.10, ...), custom_call_target="tpu_custom_call" | custom-call | flops 1 | bytes 1 | tf_op jit(solution)/shard_map/cond/branch_1_fun/inner_quarter/pallas_call | solution.py:1000
  142.8 4.0 %collective-permute-start.11 = (bf16[80,1024]{1,0:T(8,128)(2,1)}, bf16[80,1024]{1,0:T(8,128)(2,1)S(1)}, u32[]{:S(2)}, u32[]{:S(2)}) collective-permute-start(bf16[80,1024]{1,0:T(8,128)(2,1)} %get-tuple-element.97), channel_id=1, source_target_pairs={{0,16},{2,18},{4,20},{6,22},{8,24},{10,26},{12,28},{14,30},{16,0},... | collective-permute-start | bytes 491528 | tf_op jit(solution)/shard_map/cond/branch_1_fun/ppermute | solution.py:33
  146.8 1.7 collective-permute-start.12
  148.8 1.7 fusion.30
  150.6 8.1 %collective-permute-done.11 = bf16[80,1024]{1,0:T(8,128)(2,1)S(1)} collective-permute-done((bf16[80,1024]{1,0:T(8,128)(2,1)}, bf16[80,1024]{1,0:T(8,128)(2,1)S(1)}, u32[]{:S(2)}, u32[]{:S(2)}) %collective-permute-start.11) | collective-permute-done | bytes 163872 | tf_op jit(solution)/shard_map/cond/branch_1_fun/ppermute | solution.py:33
  158.7 4.1 %collective-permute-done.13 = bf16[80,1024]{1,0:T(8,128)(2,1)S(1)} collective-permute-done((bf16[80,1024]{1,0:T(8,128)(2,1)S(1)}, bf16[80,1024]{1,0:T(8,128)(2,1)S(1)}, u32[]{:S(2)}, u32[]{:S(2)}) %collective-permute-start.13) | collective-permute-done | bytes 163872 | tf_op jit(solution)/shard_map/cond/branch_1_fun/ppermute | solution.py:33
  163.0 4.2 %collective-permute-start.14 = (bf16[80,1024]{1,0:T(8,128)(2,1)S(1)}, bf16[80,1024]{1,0:T(8,128)(2,1)S(1)}, u32[]{:S(2)}, u32[]{:S(2)}) collective-permute-start(bf16[80,1024]{1,0:T(8,128)(2,1)S(1)} %pad_maximum_fusion.3), channel_id=1, source_target_pairs={{0,16},{2,18},{4,20},{6,22},{8,24},{10,26},{12,28},{14,30},{16,0},... | collective-permute-start | bytes 491528 | tf_op jit(solution)/shard_map/cond/branch_1_fun/ppermute | solution.py:33
  167.3 1.5 collective-permute-start.16
  169.4 9.3 %collective-permute-done.14 = bf16[80,1024]{1,0:T(8,128)(2,1)S(1)} collective-permute-done((bf16[80,1024]{1,0:T(8,128)(2,1)S(1)}, bf16[80,1024]{1,0:T(8,128)(2,1)S(1)}, u32[]{:S(2)}, u32[]{:S(2)}) %collective-permute-start.14) | collective-permute-done | bytes 163872 | tf_op jit(solution)/shard_map/cond/branch_1_fun/ppermute | solution.py:33
  178.8 3.3 %collective-permute-done.16 = f32[256,512]{1,0:T(8,128)S(1)} collective-permute-done((f32[256,512]{1,0:T(8,128)S(1)}, f32[256,512]{1,0:T(8,128)S(1)}, u32[]{:S(2)}, u32[]{:S(2)}) %collective-permute-start.16) | collective-permute-done | bytes 524320 | tf_op jit(solution)/shard_map/cond/branch_1_fun/ppermute | solution.py:33
  182.2 10.1 %collective-permute-done.17 = f32[256,512]{1,0:T(8,128)S(1)} collective-permute-done((f32[256,512]{1,0:T(8,128)S(1)}, f32[256,512]{1,0:T(8,128)S(1)}, u32[]{:S(2)}, u32[]{:S(2)}) %collective-permute-start.17) | collective-permute-done | bytes 524320 | tf_op jit(solution)/shard_map/cond/branch_1_fun/ppermute | solution.py:33
  192.2 1.1 fusion.15
  193.3 2.5 %collective-permute-done.15 = bf16[160,1024]{1,0:T(8,128)(2,1)S(1)} collective-permute-done((bf16[160,1024]{1,0:T(8,128)(2,1)S(1)}, bf16[160,1024]{1,0:T(8,128)(2,1)S(1)}, u32[]{:S(2)}, u32[]{:S(2)}) %collective-permute-start.15) | collective-permute-done | bytes 327712 | tf_op jit(solution)/shard_map/cond/branch_1_fun/ppermute | solution.py:33
  196.0 0.9 pad_maximum_fusion.1
  197.3 15.9 %collective-permute-done.28.rest_2_ = bf16[320,1024]{1,0:T(8,128)(2,1)S(1)} collective-permute-done((bf16[320,1024]{1,0:T(8,128)(2,1)}, bf16[320,1024]{1,0:T(8,128)(2,1)S(1)}, u32[]{:S(2)}, u32[]{:S(2)}) %collective-permute-start.28) | collective-permute-done | bytes 655392 | tf_op jit(solution)/shard_map/ppermute | solution.py:33
  213.2 2.1 collective-permute-done.29.rest_3_
  215.3 0.8 copy-done.19
  216.1 8.9 %joined.1 = (f32[1024,2,1024]{2,1,0:T(2,128)}, f32[1024,1024]{1,0:T(8,128)}, f32[64,1024]{1,0:T(8,128)}, f32[16,1024]{1,0:T(8,128)}, f32[1,1024]{1,0:T(1,128)}, ...) custom-call(s32[1]{0:T(128)} %bitcast.21.place_ref, ...), custom_call_target="tpu_custom_call" | custom-call | flops 1 | bytes 1 | tf_op jit(solution)/shard_map/joined/pallas_call | solution.py:1055
  (118 shorter events, 5.2 us)
Async XLA Ops:
  7.2 208.1 %all-reduce.3.cloned.1.call-start = ((), (), s32[]{:S(2)}) async-start(), calls=%async_computation | async-start | bytes 8388608 | tf_op jit(solution)/shard_map/psum | solution.py:1208
  7.2 11.4 %collective-permute-start.18 = (bf16[256,512]{1,0:T(8,128)(2,1)}, bf16[256,512]{1,0:T(8,128)(2,1)S(1)}, u32[]{:S(2)}, u32[]{:S(2)}) collective-permute-start(bf16[256,512]{1,0:T(8,128)(2,1)} %own_ref.1), channel_id=1, source_target_pairs={{0,1},{1,0},{2,3},{3,2},{4,5},{5,4},{6,7},{7,6},{8,9},{9,8},{10,11... | collective-permute-start | bytes 786440 | tf_op jit(solution)/shard_map/ppermute | solution.py:33
  11.6 7.0 %collective-permute-start.20 = (bf16[16,512]{1,0:T(8,128)(2,1)}, bf16[16,512]{1,0:T(8,128)(2,1)S(1)}, u32[]{:S(2)}, u32[]{:S(2)}) collective-permute-start(bf16[16,512]{1,0:T(8,128)(2,1)} %edge_rows.1), channel_id=1, source_target_pairs={{0,3},{1,2},{2,5},{3,4},{4,7},{5,6},{6,9},{7,8},{8,11},{9,10},{10,... | collective-permute-start | bytes 49160 | tf_op jit(solution)/shard_map/ppermute | solution.py:51
  13.0 5.6 %collective-permute-start.19 = (bf16[16,512]{1,0:T(8,128)(2,1)}, bf16[16,512]{1,0:T(8,128)(2,1)S(1)}, u32[]{:S(2)}, u32[]{:S(2)}) collective-permute-start(bf16[16,512]{1,0:T(8,128)(2,1)} %edge_rows.1), channel_id=1, source_target_pairs={{0,2},{2,4},{4,6},{6,8},{8,10},{10,12},{12,14},{14,16},{16,18},{18... | collective-permute-start | bytes 49160 | tf_op jit(solution)/shard_map/ppermute | solution.py:28
  17.0 12.7 %collective-permute-start.22 = (bf16[256,512]{1,0:T(8,128)(2,1)}, bf16[256,512]{1,0:T(8,128)(2,1)S(1)}, u32[]{:S(2)}, u32[]{:S(2)}) collective-permute-start(bf16[256,512]{1,0:T(8,128)(2,1)} %param.27), channel_id=1, source_target_pairs={{0,1},{1,0},{2,3},{3,2},{4,5},{5,4},{6,7},{7,6},{8,9},{9,8},{10,11... | collective-permute-start | bytes 786440 | tf_op jit(solution)/shard_map/ppermute | solution.py:33
  18.6 0.7 copy-start.25
  21.6 4.0 %copy-start.15 = (bf16[96,1024]{1,0:T(8,128)(2,1)S(1)}, bf16[96,1024]{1,0:T(8,128)(2,1)}, u32[]{:S(2)}) copy-start(bf16[96,1024]{1,0:T(8,128)(2,1)} %select_ref.1) | copy-start | bytes 589828
  21.6 4.0 %copy-start.28 = (f32[4,1024]{1,0:T(4,128)S(1)}, f32[4,1024]{1,0:T(4,128)}, u32[]{:S(2)}) copy-start(f32[4,1024]{1,0:T(4,128)} %conv_weight_ref.1) | copy-start | bytes 49156
  21.6 8.1 %copy-start.11 = (bf16[256,512]{1,0:T(8,128)(2,1)S(1)}, bf16[256,512]{1,0:T(8,128)(2,1)}, u32[]{:S(2)}) copy-start(bf16[256,512]{1,0:T(8,128)(2,1)} %param.27) | copy-start | bytes 786436
  25.6 4.2 %copy-start = (bf16[1024,1024]{1,0:T(8,128)(2,1)S(1)}, bf16[1024,1024]{1,0:T(8,128)(2,1)}, u32[]{:S(2)}) copy-start(bf16[1024,1024]{1,0:T(8,128)(2,1)} %param.25) | copy-start | bytes 6291460
  28.7 4.6 %collective-permute-start.21 = (f32[96,256]{1,0:T(8,128)S(1)}, f32[96,256]{1,0:T(8,128)S(1)}, u32[]{:S(2)}, u32[]{:S(2)}) collective-permute-start(f32[96,256]{1,0:T(8,128)S(1)} %get-tuple-element.153.selected_ref), channel_id=1, source_target_pairs={{0,1},{1,0},{2,3},{3,2},{4,5},{5,4},{6,7},{7,6},{8,9},{9,8},{10,11... | collective-permute-start | bytes 294920 | tf_op jit(solution)/shard_map/ppermute | solution.py:33
  29.7 13.6 %copy-start.5 = (bf16[256,512]{1,0:T(8,128)(2,1)}, bf16[256,512]{1,0:T(8,128)(2,1)S(1)}, u32[]{:S(2)}) copy-start(bf16[256,512]{1,0:T(8,128)(2,1)S(1)} %get-tuple-element.232) | copy-start | bytes 786436
  29.7 13.6 %copy-start.6 = (bf16[256,512]{1,0:T(8,128)(2,1)}, bf16[256,512]{1,0:T(8,128)(2,1)S(1)}, u32[]{:S(2)}) copy-start(bf16[256,512]{1,0:T(8,128)(2,1)S(1)} %get-tuple-element.233) | copy-start | bytes 786436
  29.8 3.6 %copy-start.9 = (f32[16,1024]{1,0:T(8,128)S(1)}, f32[16,1024]{1,0:T(8,128)}, u32[]{:S(2)}) copy-start(f32[16,1024]{1,0:T(8,128)} %decay_log_ref.7) | copy-start | bytes 196612
  29.8 3.6 %copy-start.20 = (bf16[64,1024]{1,0:T(8,128)(2,1)S(1)}, bf16[64,1024]{1,0:T(8,128)(2,1)}, u32[]{:S(2)}) copy-start(bf16[64,1024]{1,0:T(8,128)(2,1)} %step_weight_ref.1) | copy-start | bytes 393220
  33.4 10.0 %copy-start.14 = (f32[96,256]{1,0:T(8,128)}, f32[96,256]{1,0:T(8,128)S(1)}, u32[]{:S(2)}) copy-start(f32[96,256]{1,0:T(8,128)S(1)} %collective-permute-done.21.other_ref) | copy-start | bytes 294916
  43.4 1.7 collective-permute-start.23
  46.8 5.2 %collective-permute-start.24 = (bf16[48,1024]{1,0:T(8,128)(2,1)}, bf16[48,1024]{1,0:T(8,128)(2,1)}, u32[]{:S(2)}, u32[]{:S(2)}) collective-permute-start(bf16[48,1024]{1,0:T(8,128)(2,1)} %get-tuple-element.158.own_ref), channel_id=1, source_target_pairs={{0,4},{2,6},{4,0},{6,2},{8,12},{10,14},{12,8},{14,10},{16,20},{18,... | collective-permute-start | bytes 294920 | tf_op jit(solution)/shard_map/ppermute | solution.py:33
  53.7 8.0 %collective-permute-start.25 = (bf16[16,1024]{1,0:T(8,128)(2,1)}, bf16[16,1024]{1,0:T(8,128)(2,1)S(1)}, u32[]{:S(2)}, u32[]{:S(2)}) collective-permute-start(bf16[16,1024]{1,0:T(8,128)(2,1)} %get-tuple-element.161), channel_id=1, source_target_pairs={{0,8},{2,10},{4,12},{6,14},{8,16},{10,18},{12,20},{14,22},{16,24},... | collective-permute-start | bytes 98312 | tf_op jit(solution)/shard_map/ppermute | solution.py:28
  58.3 15.3 %collective-permute-start.26 = (bf16[16,1024]{1,0:T(8,128)(2,1)}, bf16[16,1024]{1,0:T(8,128)(2,1)S(1)}, u32[]{:S(2)}, u32[]{:S(2)}) collective-permute-start(bf16[16,1024]{1,0:T(8,128)(2,1)} %get-tuple-element.164), channel_id=1, source_target_pairs={{8,0},{10,2},{12,4},{14,6},{16,8},{18,10},{20,12},{22,14},{24,16},... | collective-permute-start | bytes 98312 | tf_op jit(solution)/shard_map/ppermute | solution.py:28
  97.2 5.0 %copy-start.13 = (f32[256,1024]{1,0:T(8,128)S(1)}, f32[256,1024]{1,0:T(8,128)}, u32[]{:S(2)}) copy-start(f32[256,1024]{1,0:T(8,128)} %get-tuple-element.79.convolved_ref) | copy-start | bytes 3145732 | tf_op jit(solution)/shard_map/cond
  97.2 5.0 %copy-start.16 = (bf16[96,1024]{1,0:T(8,128)(2,1)S(1)}, bf16[96,1024]{1,0:T(8,128)(2,1)}, u32[]{:S(2)}) copy-start(bf16[96,1024]{1,0:T(8,128)(2,1)} %get-tuple-element.77.select_ref) | copy-start | bytes 589828 | tf_op jit(solution)/shard_map/cond
  97.2 5.0 %collective-permute-start = (f32[96,256]{1,0:T(8,128)}, f32[96,256]{1,0:T(8,128)}, u32[]{:S(2)}, u32[]{:S(2)}) collective-permute-start(f32[96,256]{1,0:T(8,128)} %get-tuple-element.76.select_grad_ref.refs_1_), channel_id=1, source_target_pairs={{0,1},{1,0},{2,3},{3,2},{4,5},{5,4},{6,7},{7,6},{8,9},{9,8},{10,11... | collective-permute-start | bytes 294920 | tf_op jit(solution)/shard_map/cond/branch_1_fun/ppermute | solution.py:33
  99.5 10.1 %collective-permute-start.4 = (bf16[256,256]{1,0:T(8,128)(2,1)}, bf16[256,256]{1,0:T(8,128)(2,1)S(1)}, u32[]{:S(2)}, u32[]{:S(2)}) collective-permute-start(bf16[256,256]{1,0:T(8,128)(2,1)} %get-tuple-element.223), channel_id=1, source_target_pairs={{0,6},{2,4},{4,2},{6,0},{8,14},{10,12},{12,10},{14,8},{16,22},{18,... | collective-permute-start | bytes 393224 | tf_op jit(solution)/shard_map/cond/branch_1_fun/ppermute | solution.py:33
  99.5 10.1 %collective-permute-start.3 = (bf16[256,256]{1,0:T(8,128)(2,1)}, bf16[256,256]{1,0:T(8,128)(2,1)S(1)}, u32[]{:S(2)}, u32[]{:S(2)}) collective-permute-start(bf16[256,256]{1,0:T(8,128)(2,1)} %get-tuple-element.224), channel_id=1, source_target_pairs={{0,2},{2,0},{4,6},{6,4},{8,10},{10,8},{12,14},{14,12},{16,18},{18,... | collective-permute-start | bytes 393224 | tf_op jit(solution)/shard_map/cond/branch_1_fun/ppermute | solution.py:33
  100.2 9.4 %collective-permute-start.2 = (bf16[256,256]{1,0:T(8,128)(2,1)}, bf16[256,256]{1,0:T(8,128)(2,1)S(1)}, u32[]{:S(2)}, u32[]{:S(2)}) collective-permute-start(bf16[256,256]{1,0:T(8,128)(2,1)} %get-tuple-element.225), channel_id=1, source_target_pairs={{0,4},{2,6},{4,0},{6,2},{8,12},{10,14},{12,8},{14,10},{16,20},{18,... | collective-permute-start | bytes 393224 | tf_op jit(solution)/shard_map/cond/branch_1_fun/ppermute | solution.py:33
  102.2 5.7 %copy-start.27 = (f32[256,1]{1,0:T(8,128)S(1)}, f32[256,1]{1,0:T(8,128)}, u32[]{:S(2)}) copy-start(f32[256,1]{1,0:T(8,128)} %get-tuple-element.208) | copy-start | bytes 3076 | tf_op jit(solution)/shard_map/cond
  106.2 12.4 %copy-start.31 = (f32[1024]{0:T(1024)S(1)}, f32[1024]{0:T(1024)}, u32[]{:S(2)}) copy-start(f32[1024]{0:T(1024)} %get-tuple-element.89) | copy-start | bytes 12292 | tf_op jit(solution)/shard_map/cond
  106.2 12.4 %copy-start.36 = (bf16[256,1024]{1,0:T(8,128)(2,1)S(1)}, bf16[256,1024]{1,0:T(8,128)(2,1)}, u32[]{:S(2)}) copy-start(bf16[256,1024]{1,0:T(8,128)(2,1)} %get-tuple-element.87) | copy-start | bytes 1572868 | tf_op jit(solution)/shard_map/cond
  106.2 3.4 %collective-permute-start.1 = (f32[8,1024]{1,0:T(8,128)}, f32[8,1024]{1,0:T(8,128)S(1)}, u32[]{:S(2)}, u32[]{:S(2)}) collective-permute-start(f32[8,1024]{1,0:T(8,128)} %get-tuple-element.83), channel_id=1, source_target_pairs={{2,0},{4,2},{6,4},{8,6},{10,8},{12,10},{14,12},{16,14},{18,16},{20... | collective-permute-start | bytes 98312 | tf_op jit(solution)/shard_map/cond/branch_1_fun/ppermute | solution.py:28
  109.7 0.7 copy-start.21
  109.7 0.7 copy-start.22
  109.7 0.7 copy-start.23
  111.9 21.7 %collective-permute-start.5 = (bf16[256,1024]{1,0:T(8,128)(2,1)}, bf16[256,1024]{1,0:T(8,128)(2,1)S(1)}, u32[]{:S(2)}, u32[]{:S(2)}) collective-permute-start(bf16[256,1024]{1,0:T(8,128)(2,1)} %patched.1.wait_ref.own_ref), channel_id=1, source_target_pairs={{0,4},{2,6},{4,0},{6,2},{8,12},{10,14},{12,8},{14,10},{16,20},{18,... | collective-permute-start | bytes 1572872 | tf_op jit(solution)/shard_map/cond/branch_1_fun/ppermute | solution.py:33
  115.5 9.6 %collective-permute-start.8 = (bf16[128,1024]{1,0:T(8,128)(2,1)}, bf16[128,1024]{1,0:T(8,128)(2,1)S(1)}, u32[]{:S(2)}, u32[]{:S(2)}) collective-permute-start(bf16[128,1024]{1,0:T(8,128)(2,1)} %get-tuple-element.93), channel_id=1, source_target_pairs={{0,2},{2,0},{4,6},{6,4},{8,10},{10,8},{12,14},{14,12},{16,18},{18,... | collective-permute-start | bytes 786440 | tf_op jit(solution)/shard_map/cond/branch_1_fun/ppermute | solution.py:33
  123.0 11.5 %copy-start.2 = (bf16[256,1024]{1,0:T(8,128)(2,1)S(1)}, bf16[256,1024]{1,0:T(8,128)(2,1)}, u32[]{:S(2)}) copy-start(bf16[256,1024]{1,0:T(8,128)(2,1)} %patched.1.wait_ref.own_ref) | copy-start | bytes 1572868 | tf_op jit(solution)/shard_map/cond
  123.0 4.9 %collective-permute-start.6 = (f32[1,1024]{1,0:T(1,128)S(1)}, f32[1,1024]{1,0:T(1,128)S(1)}, u32[]{:S(2)}, u32[]{:S(2)}) collective-permute-start(f32[1,1024]{1,0:T(1,128)S(1)} %bitcast.42), channel_id=1, source_target_pairs={{0,1},{1,0},{2,3},{3,2},{4,5},{5,4},{6,7},{7,6},{8,9},{9,8},{10,11... | collective-permute-start | bytes 12296 | tf_op jit(solution)/shard_map/cond/branch_1_fun/ppermute | solution.py:33
  124.4 4.0 %collective-permute-start.7 = (f32[1,256]{1,0:T(1,128)S(1)}, f32[1,256]{1,0:T(1,128)S(1)}, u32[]{:S(2)}, u32[]{:S(2)}) collective-permute-start(f32[1,256]{1,0:T(1,128)S(1)} %bitcast.46), channel_id=1, source_target_pairs={{0,1},{1,0},{2,3},{3,2},{4,5},{5,4},{6,7},{7,6},{8,9},{9,8},{10,11... | collective-permute-start | bytes 3080 | tf_op jit(solution)/shard_map/cond/branch_1_fun/ppermute | solution.py:33
  125.1 0.7 copy-start.26
  127.7 5.9 %collective-permute-start.9 = (bf16[64,1024]{1,0:T(8,128)(2,1)}, bf16[64,1024]{1,0:T(8,128)(2,1)S(1)}, u32[]{:S(2)}, u32[]{:S(2)}) collective-permute-start(bf16[64,1024]{1,0:T(8,128)(2,1)} %get-tuple-element.94), channel_id=1, source_target_pairs={{0,4},{2,6},{4,0},{6,2},{8,12},{10,14},{12,8},{14,10},{16,20},{18,... | collective-permute-start | bytes 393224 | tf_op jit(solution)/shard_map/cond/branch_1_fun/ppermute | solution.py:33
  128.4 5.1 %copy-start.34 = (f32[1,256]{1,0:T(1,128)}, f32[1,256]{1,0:T(1,128)S(1)}, u32[]{:S(2)}) copy-start(f32[1,256]{1,0:T(1,128)S(1)} %collective-permute-done.7.refs_2_) | copy-start | bytes 3076 | tf_op jit(solution)/shard_map/cond
  133.6 0.8 copy-start.3
  135.5 2.7 %collective-permute-start.10 = (bf16[512,1024]{1,0:T(8,128)(2,1)S(1)}, bf16[512,1024]{1,0:T(8,128)(2,1)S(1)}, u32[]{:S(2)}, u32[]{:S(2)}) collective-permute-start(bf16[512,1024]{1,0:T(8,128)(2,1)S(1)} %pad_maximum_fusion), channel_id=1, source_target_pairs={{0,2},{2,0},{4,6},{6,4},{8,10},{10,8},{12,14},{14,12},{16,18},{18,... | collective-permute-start | bytes 3145736 | tf_op jit(solution)/shard_map/cond/branch_1_fun/ppermute | solution.py:33
  138.3 1.0 copy-start.10
  142.8 5.7 %copy-start.37 = (bf16[80,1024]{1,0:T(8,128)(2,1)S(1)}, bf16[80,1024]{1,0:T(8,128)(2,1)}, u32[]{:S(2)}) copy-start(bf16[80,1024]{1,0:T(8,128)(2,1)} %get-tuple-element.99) | copy-start | bytes 491524 | tf_op jit(solution)/shard_map/cond
  142.8 6.0 %copy-start.1 = (bf16[1024,1024]{1,0:T(8,128)(2,1)S(1)}, bf16[1024,1024]{1,0:T(8,128)(2,1)}, u32[]{:S(2)}) copy-start(bf16[1024,1024]{1,0:T(8,128)(2,1)} %get-tuple-element.103) | copy-start | bytes 6291460 | tf_op jit(solution)/shard_map/cond
  142.8 20.1 %copy-start.4 = (f32[80,1024]{1,0:T(8,128)S(1)}, f32[80,1024]{1,0:T(8,128)}, u32[]{:S(2)}) copy-start(f32[80,1024]{1,0:T(8,128)} %get-tuple-element.96.refs_1_) | copy-start | bytes 983044 | tf_op jit(solution)/shard_map/cond
  142.8 15.9 %collective-permute-start.11 = (bf16[80,1024]{1,0:T(8,128)(2,1)}, bf16[80,1024]{1,0:T(8,128)(2,1)S(1)}, u32[]{:S(2)}, u32[]{:S(2)}) collective-permute-start(bf16[80,1024]{1,0:T(8,128)(2,1)} %get-tuple-element.97), channel_id=1, source_target_pairs={{0,16},{2,18},{4,20},{6,22},{8,24},{10,26},{12,28},{14,30},{16,0},... | collective-permute-start | bytes 491528 | tf_op jit(solution)/shard_map/cond/branch_1_fun/ppermute | solution.py:33
  146.8 11.9 %collective-permute-start.12 = (bf16[80,1024]{1,0:T(8,128)(2,1)}, bf16[80,1024]{1,0:T(8,128)(2,1)S(1)}, u32[]{:S(2)}, u32[]{:S(2)}) collective-permute-start(bf16[80,1024]{1,0:T(8,128)(2,1)} %get-tuple-element.98), channel_id=1, source_target_pairs={{0,8},{2,10},{4,12},{6,14},{8,0},{10,2},{12,4},{14,6},{16,24},{18,... | collective-permute-start | bytes 491528 | tf_op jit(solution)/shard_map/cond/branch_1_fun/ppermute | solution.py:33
  148.5 14.3 %collective-permute-start.13 = (bf16[80,1024]{1,0:T(8,128)(2,1)S(1)}, bf16[80,1024]{1,0:T(8,128)(2,1)S(1)}, u32[]{:S(2)}, u32[]{:S(2)}) collective-permute-start(bf16[80,1024]{1,0:T(8,128)(2,1)S(1)} %copy-done.37), channel_id=1, source_target_pairs={{0,24},{2,26},{4,28},{6,30},{8,16},{10,18},{12,20},{14,22},{16,8},... | collective-permute-start | bytes 491528 | tf_op jit(solution)/shard_map/cond/branch_1_fun/ppermute | solution.py:33
  150.6 18.2 %copy-start.8 = (f32[256,512]{1,0:T(8,128)S(1)}, f32[256,512]{1,0:T(8,128)}, u32[]{:S(2)}) copy-start(f32[256,512]{1,0:T(8,128)} %after.8) | copy-start | bytes 1572868 | tf_op jit(solution)/shard_map/cond
  150.6 28.2 %copy-start.35 = (f32[1,256]{1,0:T(1,128)S(1)}, f32[1,256]{1,0:T(1,128)}, u32[]{:S(2)}) copy-start(f32[1,256]{1,0:T(1,128)} %copy-done.34) | copy-start | bytes 3076 | tf_op jit(solution)/shard_map/cond
  150.6 41.7 %copy-start.7 = (bf16[256,512]{1,0:T(8,128)(2,1)S(1)}, bf16[256,512]{1,0:T(8,128)(2,1)}, u32[]{:S(2)}) copy-start(bf16[256,512]{1,0:T(8,128)(2,1)} %get-tuple-element.100) | copy-start | bytes 786436 | tf_op jit(solution)/shard_map/cond
  150.6 41.6 %copy-start.12 = (bf16[256,512]{1,0:T(8,128)(2,1)S(1)}, bf16[256,512]{1,0:T(8,128)(2,1)}, u32[]{:S(2)}) copy-start(bf16[256,512]{1,0:T(8,128)(2,1)} %get-tuple-element.104) | copy-start | bytes 786436 | tf_op jit(solution)/shard_map/cond
  163.0 15.6 %collective-permute-start.14 = (bf16[80,1024]{1,0:T(8,128)(2,1)S(1)}, bf16[80,1024]{1,0:T(8,128)(2,1)S(1)}, u32[]{:S(2)}, u32[]{:S(2)}) collective-permute-start(bf16[80,1024]{1,0:T(8,128)(2,1)S(1)} %pad_maximum_fusion.3), channel_id=1, source_target_pairs={{0,16},{2,18},{4,20},{6,22},{8,24},{10,26},{12,28},{14,30},{16,0},... | collective-permute-start | bytes 491528 | tf_op jit(solution)/shard_map/cond/branch_1_fun/ppermute | solution.py:33
  167.3 14.9 %collective-permute-start.16 = (f32[256,512]{1,0:T(8,128)S(1)}, f32[256,512]{1,0:T(8,128)S(1)}, u32[]{:S(2)}, u32[]{:S(2)}) collective-permute-start(f32[256,512]{1,0:T(8,128)S(1)} %slice_select_fusion.1), channel_id=1, source_target_pairs={{0,1},{1,0},{2,3},{3,2},{4,5},{5,4},{6,7},{7,6},{8,9},{9,8},{10,11... | collective-permute-start | bytes 1572872 | tf_op jit(solution)/shard_map/cond/branch_1_fun/ppermute | solution.py:33
  168.8 23.5 %collective-permute-start.17 = (f32[256,512]{1,0:T(8,128)S(1)}, f32[256,512]{1,0:T(8,128)S(1)}, u32[]{:S(2)}, u32[]{:S(2)}) collective-permute-start(f32[256,512]{1,0:T(8,128)S(1)} %copy-done.8), channel_id=1, source_target_pairs={{0,1},{1,0},{2,3},{3,2},{4,5},{5,4},{6,7},{7,6},{8,9},{9,8},{10,11... | collective-permute-start | bytes 1572872 | tf_op jit(solution)/shard_map/cond/branch_1_fun/ppermute | solution.py:33
  178.7 17.1 %collective-permute-start.15 = (bf16[160,1024]{1,0:T(8,128)(2,1)S(1)}, bf16[160,1024]{1,0:T(8,128)(2,1)S(1)}, u32[]{:S(2)}, u32[]{:S(2)}) collective-permute-start(bf16[160,1024]{1,0:T(8,128)(2,1)S(1)} %pad_maximum_fusion.2), channel_id=1, source_target_pairs={{0,8},{2,10},{4,12},{6,14},{8,0},{10,2},{12,4},{14,6},{16,24},{18,... | collective-permute-start | bytes 983048 | tf_op jit(solution)/shard_map/cond/branch_1_fun/ppermute | solution.py:33
  196.9 16.3 %collective-permute-start.28 = (bf16[320,1024]{1,0:T(8,128)(2,1)}, bf16[320,1024]{1,0:T(8,128)(2,1)S(1)}, u32[]{:S(2)}, u32[]{:S(2)}) collective-permute-start(bf16[320,1024]{1,0:T(8,128)(2,1)} %get-tuple-element.174.rest_0_), channel_id=1, source_target_pairs={{0,4},{2,6},{4,0},{6,2},{8,12},{10,14},{12,8},{14,10},{16,20},{18,... | collective-permute-start | bytes 1966088 | tf_op jit(solution)/shard_map/ppermute | solution.py:33
  197.3 15.9 %collective-permute-start.27 = (bf16[320,1024]{1,0:T(8,128)(2,1)}, bf16[320,1024]{1,0:T(8,128)(2,1)S(1)}, u32[]{:S(2)}, u32[]{:S(2)}) collective-permute-start(bf16[320,1024]{1,0:T(8,128)(2,1)} %get-tuple-element.174.rest_0_), channel_id=1, source_target_pairs={{0,2},{2,0},{4,6},{6,4},{8,10},{10,8},{12,14},{14,12},{16,18},{18,... | collective-permute-start | bytes 1966088 | tf_op jit(solution)/shard_map/ppermute | solution.py:33
  213.2 2.1 copy-start.17
  213.2 2.1 collective-permute-start.29
  213.2 2.1 copy-start.18
  215.3 0.8 copy-start.19
  (5 other events, 3.1 us)
Sparse Core Ops, SparseCore 0:
  73.8 134.6 all-reduce.2

commit v24 on v19

--- a/solution.py
+++ b/solution.py
@@ -12,7 +12,7 @@
 reset_step = 1e30
 lanes = 128
 halo = 16
-body_rows = 32
+body_rows = 64
 scan_width = 512
 vmem_bytes = 56 * 1024 * 1024
 tiny_cost = pl.CostEstimate(flops=1, bytes_accessed=1, transcendentals=0)

time: 228 us -> 230 us (level)
  waiting for transfers between devices: 64.8 us -> 68.6 us
  Pallas kernels: 78.7 us -> 76.1 us
    pallas_call x5, Pallas kernels: 52 us -> 49.4 us  [call(): pl.pallas_call(kernel, grid=(width // scan_width,), in_specs=in_specs, ou...]
    ppermute x26, waiting for transfers between devices: 62.7 us -> 65.1 us  [swapped(): return lax.ppermute(array, axis, [(i, i ^ bit) for i in range(peers)])]
  transfers between devices with their start and end apart: 32 -> 32, of which waited for: 15 -> 15; matrix products, arithmetic and copies ran while one was open for 8% -> 8% of each run, Pallas kernels for 26% -> 25%
where the time goes in v24:
time: 230 us; the launch traced here: 229 us
  Pallas kernels  76.1 us (33%)
  waiting for transfers between devices  68.6 us (30%)
  starting transfers between devices  46 us (20%)
  between operations  14.3 us (6%)
  matrix products  9.89 us (4%)
  other arithmetic  7.13 us (3%)
  local copies, waits for them, and re-layouts  6.47 us (3%)
    ppermute x26, waiting for transfers between devices, swapped(): return lax.ppermute(array, axis, [(i, i ^ bit) for i in range(peers)])  65.1 us
    pallas_call x5, Pallas kernels, call(): pl.pallas_call(kernel, grid=(width // scan_width,), in_specs=in_specs, ou...  49.4 us
    ppermute x26, starting transfers between devices, swapped(): return lax.ppermute(array, axis, [(i, i ^ bit) for i in range(peers)])  33 us
    ppermute x4, starting transfers between devices, passed_along(): return lax.ppermute(array, axis, pairs)  11.7 us
    pallas_call x2, Pallas kernels, joined(): pl.pallas_call(kernel, grid_spec=pltpu.PrefetchScalarGridSpec(num_scalar_...  10.5 us
  transfers between devices with their start and end apart: 32, of which 15 were waited for; matrix products, arithmetic and copies ran while one was open for 8% of the time, Pallas kernels for 25%

profile of v24, /device:TPU:0, one launch (start us, length us, event | category | flops | bytes accessed | tf_op | source)
XLA Modules:
  0.0 228.8 jit_solution(8511280243331702240)
XLA Ops:
  7.2 3.0 %collective-permute-start.19 = (bf16[256,512]{1,0:T(8,128)(2,1)}, bf16[256,512]{1,0:T(8,128)(2,1)S(1)}, u32[]{:S(2)}, u32[]{:S(2)}) collective-permute-start(bf16[256,512]{1,0:T(8,128)(2,1)} %own_ref.1), channel_id=1, source_target_pairs={{0,1},{1,0},{2,3},{3,2},{4,5},{5,4},{6,7},{7,6},{8,9},{9,8},{10,11... | collective-permute-start | bytes 786440 | tf_op jit(solution)/shard_map/ppermute | solution.py:33
  10.3 1.4 edge_rows.1
  11.6 1.3 collective-permute-start.21
  13.0 4.0 %collective-permute-start.20 = (bf16[16,512]{1,0:T(8,128)(2,1)}, bf16[16,512]{1,0:T(8,128)(2,1)S(1)}, u32[]{:S(2)}, u32[]{:S(2)}) collective-permute-start(bf16[16,512]{1,0:T(8,128)(2,1)} %edge_rows.1), channel_id=1, source_target_pairs={{0,2},{2,4},{4,6},{6,8},{8,10},{10,12},{12,14},{14,16},{16,18},{18... | collective-permute-start | bytes 49160 | tf_op jit(solution)/shard_map/ppermute | solution.py:28
  17.0 1.6 collective-permute-start.23
  19.3 2.3 normalized.1
  21.6 4.0 %fusion.25.inner_ref.gate_ref = bf16[2,272,1024]{2,1,0:T(8,128)(2,1)S(1)} fusion(bf16[1024,2,1024]{2,1,0:T(2,128)(2,1)} %param.17, bf16[272,1024]{1,0:T(8,128)(2,1)} %get-tuple-element.152), kind=kOutput, calls=%fused_computation.47 | convolution fusion | flops 1141407744 | bytes 5865472 | tf_op jit(solution)/shard_map/td,dce->cte/dot_general | solution.py:1212
  25.6 3.1 %convolve.1 = (f32[256,1024]{1,0:T(8,128)}, bf16[256,1024]{1,0:T(8,128)(2,1)S(1)}, f32[96,256]{1,0:T(8,128)S(1)}) custom-call(bf16[2,272,1024]{2,1,0:T(8,128)(2,1)S(1)} %fusion.25.inner_ref.gate_ref, f32[4,1024]{1,0:T(4,128)S(1)} %copy-done.30, f32[1,1024]{1,0:T(1,128)} %bitcast.40, bf16[96,1024]{1,0:T(8,128)(2,1)S(1)} %copy-done.21, ...), custom_call_target="tpu_custom_call" | custom-call | flops 1 | bytes 1 | tf_op jit(solution)/shard_map/convolve/pallas_call | solution.py:127
  28.7 0.9 collective-permute-start.22
  29.8 0.7 fusion.29.gated_grad_ref
  30.5 2.8 %collective-permute-done.22.other_ref = f32[96,256]{1,0:T(8,128)S(1)} collective-permute-done((f32[96,256]{1,0:T(8,128)S(1)}, f32[96,256]{1,0:T(8,128)S(1)}, u32[]{:S(2)}, u32[]{:S(2)}) %collective-permute-start.22) | collective-permute-done | bytes 98336 | tf_op jit(solution)/shard_map/ppermute | solution.py:33
  33.4 9.4 %scan_ends.1 = (f32[256,1024]{1,0:T(8,128)}, f32[256,1024]{1,0:T(8,128)}, bf16[48,1024]{1,0:T(8,128)(2,1)}) custom-call(f32[96,256]{1,0:T(8,128)S(1)} %get-tuple-element.154.selected_ref, f32[96,256]{1,0:T(8,128)S(1)} %collective-permute-done.22.other_ref, bf16[64,1024]{1,0:T(8,128)(2,1)S(1)} %copy-done.22, f32[1,1024]{1,0:T(1,128)} %bitcast.41, ...), custom_call_target="tpu_custom_call" | custom-call | flops 1 | bytes 1 | tf_op jit(solution)/shard_map/scan_ends/pallas_call | solution.py:127
  42.9 1.6 collective-permute-done.24.other_ref
  44.5 1.7 carry_round.2
  46.2 1.7 collective-permute-start.25
  47.9 3.5 %collective-permute-done.25.other_ref = bf16[48,1024]{1,0:T(8,128)(2,1)} collective-permute-done((bf16[48,1024]{1,0:T(8,128)(2,1)}, bf16[48,1024]{1,0:T(8,128)(2,1)}, u32[]{:S(2)}, u32[]{:S(2)}) %collective-permute-start.25) | collective-permute-done | bytes 98336 | tf_op jit(solution)/shard_map/ppermute | solution.py:33
  51.4 1.8 carry_round.3
  53.2 4.6 %collective-permute-start.26 = (bf16[16,1024]{1,0:T(8,128)(2,1)}, bf16[16,1024]{1,0:T(8,128)(2,1)S(1)}, u32[]{:S(2)}, u32[]{:S(2)}) collective-permute-start(bf16[16,1024]{1,0:T(8,128)(2,1)} %get-tuple-element.162), channel_id=1, source_target_pairs={{0,8},{2,10},{4,12},{6,14},{8,16},{10,18},{12,20},{14,22},{16,24},... | collective-permute-start | bytes 98312 | tf_op jit(solution)/shard_map/ppermute | solution.py:28
  57.7 1.5 collective-permute-start.27
  59.2 1.9 pad_maximum_fusion.5.cot_ref
  61.8 10.3 %scan_forward.1 = (bf16[256,1024]{1,0:T(8,128)(2,1)}, bf16[256,1024]{1,0:T(8,128)(2,1)}, bf16[1024,1024]{1,0:T(8,128)(2,1)}, bf16[1024,1024]{1,0:T(8,128)(2,1)}, f32[16,1024]{1,0:T(8,128)}) custom-call(f32[96,256]{1,0:T(8,128)S(1)} %get-tuple-element.154.selected_ref, f32[96,256]{1,0:T(8,128)} %copy-done.20, f32[256,1024]{1,0:T(8,128)} %get-tuple-element.157.step_ref, ...), custom_call_target="tpu_custom_call" | custom-call | flops 1 | bytes 1 | tf_op jit(solution)/shard_map/scan_forward/pallas_call | solution.py:127
  72.2 119.1 %conditional.1 = (bf16[320,1024]{1,0:T(8,128)(2,1)S(1)}, bf16[256,512]{1,0:T(8,128)(2,1)}, bf16[256,512]{1,0:T(8,128)(2,1)}) conditional(s32[]{:T(128)} %convert_element_type.43, () %tuple.16, (s32[]{:T(128)}, f32[1024]{0:T(1024)}, f32[96,256]{1,0:T(8,128)S(1)}, f32[96,256]{1,0:T(8,128)}, f32[256,1024]{1,0:T(8,128)}, ...), branch_computations={%region_0.1_spmd, %region_1.4_spmd} | conditional | flops 1621776640 | bytes 85911368 | solution.py:1343
  72.2 22.5 %scan_backward.1 = (f32[256,1024]{1,0:T(8,128)}, f32[96,256]{1,0:T(8,128)}, f32[82,1024]{1,0:T(8,128)}) custom-call(f32[96,256]{1,0:T(8,128)S(1)} %get-tuple-element.62.selected_ref, f32[96,256]{1,0:T(8,128)} %get-tuple-element.63.other_ref, f32[256,1024]{1,0:T(8,128)} %get-tuple-element.64.step_pre_ref, f32[256,1024]{1,0:T(8,128)} %get-tuple-element.65.step_ref, ...), custom_call_target="tpu_custom_call" | custom-call | flops 1 | bytes 1 | tf_op jit(solution)/shard_map/cond/branch_1_fun/scan_backward/pallas_call | solution.py:127
  94.7 1.5 collective-permute-start
  96.2 0.8 constant_dynamic-slice_fusion
  97.0 0.7 collective-permute-start.3
  97.7 1.4 collective-permute-start.2
  99.7 4.0 %convolve_grad.1 = (bf16[256,1024]{1,0:T(8,128)(2,1)}, f32[8,1024]{1,0:T(8,128)}, f32[8,1024]{1,0:T(8,128)}, f32[101,1024]{1,0:T(8,128)}) custom-call(f32[96,256]{1,0:T(8,128)} %get-tuple-element.76.select_grad_ref.refs_1_, f32[96,256]{1,0:T(8,128)} %collective-permute-done.other_ref, bf16[96,1024]{1,0:T(8,128)(2,1)} %get-tuple-element.77.select_ref, ...), custom_call_target="tpu_custom_call" | custom-call | flops 1 | bytes 1 | tf_op jit(solution)/shard_map/cond/branch_1_fun/convolve_grad/pallas_call | solution.py:127
  103.7 1.6 collective-permute-start.1
  105.5 1.7 collective-permute-done.1.next_ref
  108.0 1.4 patched.1.wait_ref.own_ref
  109.4 1.2 collective-permute-start.5
  110.7 2.2 small_halves.1
  112.9 3.0 %collective-permute-start.8 = (bf16[128,1024]{1,0:T(8,128)(2,1)}, bf16[128,1024]{1,0:T(8,128)(2,1)S(1)}, u32[]{:S(2)}, u32[]{:S(2)}) collective-permute-start(bf16[128,1024]{1,0:T(8,128)(2,1)} %get-tuple-element.93), channel_id=1, source_target_pairs={{0,2},{2,0},{4,6},{6,4},{8,10},{10,8},{12,14},{14,12},{16,18},{18,... | collective-permute-start | bytes 786440 | tf_op jit(solution)/shard_map/cond/branch_1_fun/ppermute | solution.py:33
  115.8 4.5 %fusion.7 = (f32[256]{0:T(256)S(1)}, f32[1024]{0:T(1024)S(1)}, f32[256,1024]{1,0:T(8,128)S(1)}) fusion(bf16[256,1024]{1,0:T(8,128)(2,1)} %get-tuple-element.87, f32[1024]{0:T(1024)S(1)} %copy-done.33, f32[256]{0:T(256)S(1)} %bitcast.38, bf16[1024,2,1024]{2,1,0:T(2,128)(2,1)} %get-tuple-element.208, bf16[1,256,1024]{2,1,0:T(8,128)(2,1)} %bitcast.48, ...), kind=kOutput, calls=%fused_computation.7 | convolution fusion | flops 1076099840 | bytes 6825984 | tf_op jit(solution)/shard_map/cond/branch_1_fun/cte,dce->td/dot_general | solution.py:1296
  120.3 1.7 collective-permute-start.6
  122.4 0.7 copy-done.28
  123.1 1.9 folded.1
  126.1 5.0 %collective-permute-done.9.refs_3_.arrived_ref = bf16[64,1024]{1,0:T(8,128)(2,1)S(1)} collective-permute-done((bf16[64,1024]{1,0:T(8,128)(2,1)}, bf16[64,1024]{1,0:T(8,128)(2,1)S(1)}, u32[]{:S(2)}, u32[]{:S(2)}) %collective-permute-start.9) | collective-permute-done | bytes 131104 | tf_op jit(solution)/shard_map/cond/branch_1_fun/ppermute | solution.py:33
  131.9 2.1 pad_maximum_fusion
  134.1 0.9 slice_select_fusion.refs_0_
  135.0 2.0 collective-permute-done.10.far_ref
  136.9 1.0 copy-done.16
  137.9 3.5 %inner_quarter.1 = (f32[80,1024]{1,0:T(8,128)}, bf16[80,1024]{1,0:T(8,128)(2,1)}, bf16[80,1024]{1,0:T(8,128)(2,1)}, bf16[80,1024]{1,0:T(8,128)(2,1)}) custom-call(s32[1]{0:T(128)} %bitcast.place_ref, bf16[256,1024]{1,0:T(8,128)(2,1)} %patched.1.wait_ref.own_ref, bf16[256,1024]{1,0:T(8,128)(2,1)} %after.6.near_ref, bf16[512,1024]{1,0:T(8,128)(2,1)} %copy-done.16, ...), custom_call_target="tpu_custom_call" | custom-call | flops 1 | bytes 1 | tf_op jit(solution)/shard_map/cond/branch_1_fun/inner_quarter/pallas_call | solution.py:1000
  141.5 2.7 %collective-permute-start.11 = (bf16[80,1024]{1,0:T(8,128)(2,1)}, bf16[80,1024]{1,0:T(8,128)(2,1)S(1)}, u32[]{:S(2)}, u32[]{:S(2)}) collective-permute-start(bf16[80,1024]{1,0:T(8,128)(2,1)} %get-tuple-element.97), channel_id=1, source_target_pairs={{0,8},{2,10},{4,12},{6,14},{8,0},{10,2},{12,4},{14,6},{16,24},{18,... | collective-permute-start | bytes 491528 | tf_op jit(solution)/shard_map/cond/branch_1_fun/ppermute | solution.py:33
  144.2 2.9 %collective-permute-start.12 = (bf16[80,1024]{1,0:T(8,128)(2,1)S(1)}, bf16[80,1024]{1,0:T(8,128)(2,1)S(1)}, u32[]{:S(2)}, u32[]{:S(2)}) collective-permute-start(bf16[80,1024]{1,0:T(8,128)(2,1)S(1)} %copy-done.40), channel_id=1, source_target_pairs={{0,16},{2,18},{4,20},{6,22},{8,24},{10,26},{12,28},{14,30},{16,0},... | collective-permute-start | bytes 491528 | tf_op jit(solution)/shard_map/cond/branch_1_fun/ppermute | solution.py:33
  147.4 0.7 fusion.30
  148.2 8.2 %collective-permute-done.11 = bf16[80,1024]{1,0:T(8,128)(2,1)S(1)} collective-permute-done((bf16[80,1024]{1,0:T(8,128)(2,1)}, bf16[80,1024]{1,0:T(8,128)(2,1)S(1)}, u32[]{:S(2)}, u32[]{:S(2)}) %collective-permute-start.11) | collective-permute-done | bytes 163872 | tf_op jit(solution)/shard_map/cond/branch_1_fun/ppermute | solution.py:33
  156.4 5.2 %collective-permute-done.13 = bf16[80,1024]{1,0:T(8,128)(2,1)S(1)} collective-permute-done((bf16[80,1024]{1,0:T(8,128)(2,1)S(1)}, bf16[80,1024]{1,0:T(8,128)(2,1)S(1)}, u32[]{:S(2)}, u32[]{:S(2)}) %collective-permute-start.13) | collective-permute-done | bytes 163872 | tf_op jit(solution)/shard_map/cond/branch_1_fun/ppermute | solution.py:33
  161.7 3.7 %collective-permute-start.16 = (bf16[80,1024]{1,0:T(8,128)(2,1)S(1)}, bf16[80,1024]{1,0:T(8,128)(2,1)S(1)}, u32[]{:S(2)}, u32[]{:S(2)}) collective-permute-start(bf16[80,1024]{1,0:T(8,128)(2,1)S(1)} %pad_maximum_fusion.4), channel_id=1, source_target_pairs={{0,8},{2,10},{4,12},{6,14},{8,0},{10,2},{12,4},{14,6},{16,24},{18,... | collective-permute-start | bytes 491528 | tf_op jit(solution)/shard_map/cond/branch_1_fun/ppermute | solution.py:33
  165.6 1.5 collective-permute-start.17
  167.6 0.8 collective-permute-start.15
  168.5 1.6 collective-permute-start.14
  170.0 2.9 %collective-permute-done.16 = bf16[80,1024]{1,0:T(8,128)(2,1)S(1)} collective-permute-done((bf16[80,1024]{1,0:T(8,128)(2,1)S(1)}, bf16[80,1024]{1,0:T(8,128)(2,1)S(1)}, u32[]{:S(2)}, u32[]{:S(2)}) %collective-permute-start.16) | collective-permute-done | bytes 163872 | tf_op jit(solution)/shard_map/cond/branch_1_fun/ppermute | solution.py:33
  173.0 11.5 %collective-permute-done.15 = bf16[80,1024]{1,0:T(8,128)(2,1)S(1)} collective-permute-done((bf16[80,1024]{1,0:T(8,128)(2,1)S(1)}, bf16[80,1024]{1,0:T(8,128)(2,1)S(1)}, u32[]{:S(2)}, u32[]{:S(2)}) %collective-permute-start.15) | collective-permute-done | bytes 163872 | tf_op jit(solution)/shard_map/cond/branch_1_fun/ppermute | solution.py:33
  184.4 2.7 %collective-permute-done.14 = bf16[80,1024]{1,0:T(8,128)(2,1)S(1)} collective-permute-done((bf16[80,1024]{1,0:T(8,128)(2,1)S(1)}, bf16[80,1024]{1,0:T(8,128)(2,1)S(1)}, u32[]{:S(2)}, u32[]{:S(2)}) %collective-permute-start.14) | collective-permute-done | bytes 163872 | tf_op jit(solution)/shard_map/cond/branch_1_fun/ppermute | solution.py:33
  187.4 2.8 %collective-permute-done.18 = f32[256,512]{1,0:T(8,128)S(1)} collective-permute-done((f32[256,512]{1,0:T(8,128)S(1)}, f32[256,512]{1,0:T(8,128)S(1)}, u32[]{:S(2)}, u32[]{:S(2)}) %collective-permute-start.18) | collective-permute-done | bytes 524320 | tf_op jit(solution)/shard_map/cond/branch_1_fun/ppermute | solution.py:33
  190.2 1.0 fusion.15
  191.2 1.1 collective-permute-start.28
  192.3 16.5 %collective-permute-done.28.first_ref.rest_2_ = bf16[320,1024]{1,0:T(8,128)(2,1)S(1)} collective-permute-done((bf16[320,1024]{1,0:T(8,128)(2,1)S(1)}, bf16[320,1024]{1,0:T(8,128)(2,1)S(1)}, u32[]{:S(2)}, u32[]{:S(2)}) %collective-permute-start.28) | collective-permute-done | bytes 655392 | tf_op jit(solution)/shard_map/ppermute | solution.py:33
  208.8 1.8 all-reduce.3.cloned.1.call-done
  210.6 5.4 %joined.2 = (f32[1024,2,1024]{2,1,0:T(2,128)}, f32[1024,1024]{1,0:T(8,128)}) custom-call(s32[1]{0:T(128)} %bitcast.21.place_ref, bf16[1024,1024]{1,0:T(8,128)(2,1)} %get-tuple-element.219.gate_ref, bf16[320,1024]{1,0:T(8,128)(2,1)S(1)} %get-tuple-element.174.first_ref.rest_0_, bf16[320,1024]{1,0:T(8,128)(2,1)} %copy-done.9, ...), custom_call_target="tpu_custom_call" | custom-call | flops 1 | bytes 1 | tf_op jit(solution)/shard_map/joined/pallas_call | solution.py:1070
  216.1 0.8 copy-done.8
  216.9 5.0 %joined.3 = (f32[1024,2,1024]{2,1,0:T(2,128)}, f32[64,1024]{1,0:T(8,128)}, f32[16,1024]{1,0:T(8,128)}, f32[1,1024]{1,0:T(1,128)}, f32[1,1024]{1,0:T(1,128)}, /*i...) custom-call(s32[1]{0:T(128)} %bitcast.21.place_ref, ...), custom_call_target="tpu_custom_call", output_to_operand_aliasing={{0}: (8, {})} | custom-call | flops 1 | bytes 1 | tf_op jit(solution)/shard_map/joined/pallas_call | solution.py:1070
  (127 shorter events, 6.8 us)
Async XLA Ops:
  7.2 203.4 %all-reduce.3.cloned.1.call-start = ((), (), s32[]{:S(2)}) async-start(), calls=%async_computation | async-start | bytes 8388608 | tf_op jit(solution)/shard_map/psum | solution.py:1251
  7.2 11.4 %collective-permute-start.19 = (bf16[256,512]{1,0:T(8,128)(2,1)}, bf16[256,512]{1,0:T(8,128)(2,1)S(1)}, u32[]{:S(2)}, u32[]{:S(2)}) collective-permute-start(bf16[256,512]{1,0:T(8,128)(2,1)} %own_ref.1), channel_id=1, source_target_pairs={{0,1},{1,0},{2,3},{3,2},{4,5},{5,4},{6,7},{7,6},{8,9},{9,8},{10,11... | collective-permute-start | bytes 786440 | tf_op jit(solution)/shard_map/ppermute | solution.py:33
  11.6 7.0 %collective-permute-start.21 = (bf16[16,512]{1,0:T(8,128)(2,1)}, bf16[16,512]{1,0:T(8,128)(2,1)S(1)}, u32[]{:S(2)}, u32[]{:S(2)}) collective-permute-start(bf16[16,512]{1,0:T(8,128)(2,1)} %edge_rows.1), channel_id=1, source_target_pairs={{0,3},{1,2},{2,5},{3,4},{4,7},{5,6},{6,9},{7,8},{8,11},{9,10},{10,... | collective-permute-start | bytes 49160 | tf_op jit(solution)/shard_map/ppermute | solution.py:51
  13.0 5.6 %collective-permute-start.20 = (bf16[16,512]{1,0:T(8,128)(2,1)}, bf16[16,512]{1,0:T(8,128)(2,1)S(1)}, u32[]{:S(2)}, u32[]{:S(2)}) collective-permute-start(bf16[16,512]{1,0:T(8,128)(2,1)} %edge_rows.1), channel_id=1, source_target_pairs={{0,2},{2,4},{4,6},{6,8},{8,10},{10,12},{12,14},{14,16},{16,18},{18... | collective-permute-start | bytes 49160 | tf_op jit(solution)/shard_map/ppermute | solution.py:28
  17.0 12.7 %collective-permute-start.23 = (bf16[256,512]{1,0:T(8,128)(2,1)}, bf16[256,512]{1,0:T(8,128)(2,1)S(1)}, u32[]{:S(2)}, u32[]{:S(2)}) collective-permute-start(bf16[256,512]{1,0:T(8,128)(2,1)} %param.27), channel_id=1, source_target_pairs={{0,1},{1,0},{2,3},{3,2},{4,5},{5,4},{6,7},{7,6},{8,9},{9,8},{10,11... | collective-permute-start | bytes 786440 | tf_op jit(solution)/shard_map/ppermute | solution.py:33
  21.6 4.0 %copy-start.21 = (bf16[96,1024]{1,0:T(8,128)(2,1)S(1)}, bf16[96,1024]{1,0:T(8,128)(2,1)}, u32[]{:S(2)}) copy-start(bf16[96,1024]{1,0:T(8,128)(2,1)} %select_ref.1) | copy-start | bytes 589828
  21.6 4.0 %copy-start.30 = (f32[4,1024]{1,0:T(4,128)S(1)}, f32[4,1024]{1,0:T(4,128)}, u32[]{:S(2)}) copy-start(f32[4,1024]{1,0:T(4,128)} %conv_weight_ref.1) | copy-start | bytes 49156
  21.6 8.1 %copy-start.17 = (bf16[256,512]{1,0:T(8,128)(2,1)S(1)}, bf16[256,512]{1,0:T(8,128)(2,1)}, u32[]{:S(2)}) copy-start(bf16[256,512]{1,0:T(8,128)(2,1)} %param.27) | copy-start | bytes 786436
  25.6 4.2 %copy-start = (bf16[1024,1024]{1,0:T(8,128)(2,1)S(1)}, bf16[1024,1024]{1,0:T(8,128)(2,1)}, u32[]{:S(2)}) copy-start(bf16[1024,1024]{1,0:T(8,128)(2,1)} %param.25) | copy-start | bytes 6291460
  28.7 4.6 %collective-permute-start.22 = (f32[96,256]{1,0:T(8,128)S(1)}, f32[96,256]{1,0:T(8,128)S(1)}, u32[]{:S(2)}, u32[]{:S(2)}) collective-permute-start(f32[96,256]{1,0:T(8,128)S(1)} %get-tuple-element.154.selected_ref), channel_id=1, source_target_pairs={{0,1},{1,0},{2,3},{3,2},{4,5},{5,4},{6,7},{7,6},{8,9},{9,8},{10,11... | collective-permute-start | bytes 294920 | tf_op jit(solution)/shard_map/ppermute | solution.py:33
  29.7 13.1 %copy-start.10 = (bf16[256,512]{1,0:T(8,128)(2,1)}, bf16[256,512]{1,0:T(8,128)(2,1)S(1)}, u32[]{:S(2)}) copy-start(bf16[256,512]{1,0:T(8,128)(2,1)S(1)} %get-tuple-element.236) | copy-start | bytes 786436
  29.7 13.0 %copy-start.11 = (bf16[256,512]{1,0:T(8,128)(2,1)}, bf16[256,512]{1,0:T(8,128)(2,1)S(1)}, u32[]{:S(2)}) copy-start(bf16[256,512]{1,0:T(8,128)(2,1)S(1)} %get-tuple-element.237) | copy-start | bytes 786436
  29.7 3.6 %copy-start.15 = (f32[16,1024]{1,0:T(8,128)S(1)}, f32[16,1024]{1,0:T(8,128)}, u32[]{:S(2)}) copy-start(f32[16,1024]{1,0:T(8,128)} %decay_log_ref.7) | copy-start | bytes 196612
  29.8 3.6 %copy-start.22 = (bf16[64,1024]{1,0:T(8,128)(2,1)S(1)}, bf16[64,1024]{1,0:T(8,128)(2,1)}, u32[]{:S(2)}) copy-start(bf16[64,1024]{1,0:T(8,128)(2,1)} %step_weight_ref.1) | copy-start | bytes 393220
  33.4 9.4 %copy-start.20 = (f32[96,256]{1,0:T(8,128)}, f32[96,256]{1,0:T(8,128)S(1)}, u32[]{:S(2)}) copy-start(f32[96,256]{1,0:T(8,128)S(1)} %collective-permute-done.22.other_ref) | copy-start | bytes 294916
  42.8 1.7 collective-permute-start.24
  46.2 5.2 %collective-permute-start.25 = (bf16[48,1024]{1,0:T(8,128)(2,1)}, bf16[48,1024]{1,0:T(8,128)(2,1)}, u32[]{:S(2)}, u32[]{:S(2)}) collective-permute-start(bf16[48,1024]{1,0:T(8,128)(2,1)} %get-tuple-element.159.own_ref), channel_id=1, source_target_pairs={{0,4},{2,6},{4,0},{6,2},{8,12},{10,14},{12,8},{14,10},{16,20},{18,... | collective-permute-start | bytes 294920 | tf_op jit(solution)/shard_map/ppermute | solution.py:33
  53.2 8.0 %collective-permute-start.26 = (bf16[16,1024]{1,0:T(8,128)(2,1)}, bf16[16,1024]{1,0:T(8,128)(2,1)S(1)}, u32[]{:S(2)}, u32[]{:S(2)}) collective-permute-start(bf16[16,1024]{1,0:T(8,128)(2,1)} %get-tuple-element.162), channel_id=1, source_target_pairs={{0,8},{2,10},{4,12},{6,14},{8,16},{10,18},{12,20},{14,22},{16,24},... | collective-permute-start | bytes 98312 | tf_op jit(solution)/shard_map/ppermute | solution.py:28
  57.7 14.4 %collective-permute-start.27 = (bf16[16,1024]{1,0:T(8,128)(2,1)}, bf16[16,1024]{1,0:T(8,128)(2,1)S(1)}, u32[]{:S(2)}, u32[]{:S(2)}) collective-permute-start(bf16[16,1024]{1,0:T(8,128)(2,1)} %get-tuple-element.165), channel_id=1, source_target_pairs={{8,0},{10,2},{12,4},{14,6},{16,8},{18,10},{20,12},{22,14},{24,16},... | collective-permute-start | bytes 98312 | tf_op jit(solution)/shard_map/ppermute | solution.py:28
  94.7 5.0 %copy-start.19 = (f32[256,1024]{1,0:T(8,128)S(1)}, f32[256,1024]{1,0:T(8,128)}, u32[]{:S(2)}) copy-start(f32[256,1024]{1,0:T(8,128)} %get-tuple-element.79.convolved_ref) | copy-start | bytes 3145732 | tf_op jit(solution)/shard_map/cond
  94.7 5.0 %collective-permute-start = (f32[96,256]{1,0:T(8,128)}, f32[96,256]{1,0:T(8,128)}, u32[]{:S(2)}, u32[]{:S(2)}) collective-permute-start(f32[96,256]{1,0:T(8,128)} %get-tuple-element.76.select_grad_ref.refs_1_), channel_id=1, source_target_pairs={{0,1},{1,0},{2,3},{3,2},{4,5},{5,4},{6,7},{7,6},{8,9},{9,8},{10,11... | collective-permute-start | bytes 294920 | tf_op jit(solution)/shard_map/cond/branch_1_fun/ppermute | solution.py:33
  97.0 10.1 %collective-permute-start.4 = (bf16[256,256]{1,0:T(8,128)(2,1)}, bf16[256,256]{1,0:T(8,128)(2,1)S(1)}, u32[]{:S(2)}, u32[]{:S(2)}) collective-permute-start(bf16[256,256]{1,0:T(8,128)(2,1)} %get-tuple-element.225), channel_id=1, source_target_pairs={{0,6},{2,4},{4,2},{6,0},{8,14},{10,12},{12,10},{14,8},{16,22},{18,... | collective-permute-start | bytes 393224 | tf_op jit(solution)/shard_map/cond/branch_1_fun/ppermute | solution.py:33
  97.0 10.1 %collective-permute-start.3 = (bf16[256,256]{1,0:T(8,128)(2,1)}, bf16[256,256]{1,0:T(8,128)(2,1)S(1)}, u32[]{:S(2)}, u32[]{:S(2)}) collective-permute-start(bf16[256,256]{1,0:T(8,128)(2,1)} %get-tuple-element.226), channel_id=1, source_target_pairs={{0,2},{2,0},{4,6},{6,4},{8,10},{10,8},{12,14},{14,12},{16,18},{18,... | collective-permute-start | bytes 393224 | tf_op jit(solution)/shard_map/cond/branch_1_fun/ppermute | solution.py:33
  97.7 9.5 %collective-permute-start.2 = (bf16[256,256]{1,0:T(8,128)(2,1)}, bf16[256,256]{1,0:T(8,128)(2,1)S(1)}, u32[]{:S(2)}, u32[]{:S(2)}) collective-permute-start(bf16[256,256]{1,0:T(8,128)(2,1)} %get-tuple-element.227), channel_id=1, source_target_pairs={{0,4},{2,6},{4,0},{6,2},{8,12},{10,14},{12,8},{14,10},{16,20},{18,... | collective-permute-start | bytes 393224 | tf_op jit(solution)/shard_map/cond/branch_1_fun/ppermute | solution.py:33
  99.7 5.7 %copy-start.29 = (f32[256,1]{1,0:T(8,128)S(1)}, f32[256,1]{1,0:T(8,128)}, u32[]{:S(2)}) copy-start(f32[256,1]{1,0:T(8,128)} %get-tuple-element.210) | copy-start | bytes 3076 | tf_op jit(solution)/shard_map/cond
  99.7 8.3 %copy-start.36 = (s32[256]{0:T(256)S(1)}, s32[256]{0:T(256)}, u32[]{:S(2)}) copy-start(s32[256]{0:T(256)} %get-tuple-element.61.ids_ref) | copy-start | bytes 3076 | tf_op jit(solution)/shard_map/cond
  103.7 12.1 %copy-start.33 = (f32[1024]{0:T(1024)S(1)}, f32[1024]{0:T(1024)}, u32[]{:S(2)}) copy-start(f32[1024]{0:T(1024)} %get-tuple-element.89) | copy-start | bytes 12292 | tf_op jit(solution)/shard_map/cond
  103.7 3.4 %collective-permute-start.1 = (f32[8,1024]{1,0:T(8,128)}, f32[8,1024]{1,0:T(8,128)S(1)}, u32[]{:S(2)}, u32[]{:S(2)}) collective-permute-start(f32[8,1024]{1,0:T(8,128)} %get-tuple-element.83), channel_id=1, source_target_pairs={{2,0},{4,2},{6,4},{8,6},{10,8},{12,10},{14,12},{16,14},{18,16},{20... | collective-permute-start | bytes 98312 | tf_op jit(solution)/shard_map/cond/branch_1_fun/ppermute | solution.py:28
  107.2 0.8 copy-start.25
  109.4 21.7 %collective-permute-start.5 = (bf16[256,1024]{1,0:T(8,128)(2,1)}, bf16[256,1024]{1,0:T(8,128)(2,1)S(1)}, u32[]{:S(2)}, u32[]{:S(2)}) collective-permute-start(bf16[256,1024]{1,0:T(8,128)(2,1)} %patched.1.wait_ref.own_ref), channel_id=1, source_target_pairs={{0,4},{2,6},{4,0},{6,2},{8,12},{10,14},{12,8},{14,10},{16,20},{18,... | collective-permute-start | bytes 1572872 | tf_op jit(solution)/shard_map/cond/branch_1_fun/ppermute | solution.py:33
  112.9 9.6 %collective-permute-start.8 = (bf16[128,1024]{1,0:T(8,128)(2,1)}, bf16[128,1024]{1,0:T(8,128)(2,1)S(1)}, u32[]{:S(2)}, u32[]{:S(2)}) collective-permute-start(bf16[128,1024]{1,0:T(8,128)(2,1)} %get-tuple-element.93), channel_id=1, source_target_pairs={{0,2},{2,0},{4,6},{6,4},{8,10},{10,8},{12,14},{14,12},{16,18},{18,... | collective-permute-start | bytes 786440 | tf_op jit(solution)/shard_map/cond/branch_1_fun/ppermute | solution.py:33
  120.3 16.6 %copy-start.4 = (f32[256,1024]{1,0:T(8,128)}, f32[256,1024]{1,0:T(8,128)S(1)}, u32[]{:S(2)}) copy-start(f32[256,1024]{1,0:T(8,128)S(1)} %get-tuple-element.235) | copy-start | bytes 3145732 | tf_op jit(solution)/shard_map/cond
  120.3 11.6 %copy-start.2 = (bf16[256,1024]{1,0:T(8,128)(2,1)S(1)}, bf16[256,1024]{1,0:T(8,128)(2,1)}, u32[]{:S(2)}) copy-start(bf16[256,1024]{1,0:T(8,128)(2,1)} %patched.1.wait_ref.own_ref) | copy-start | bytes 1572868 | tf_op jit(solution)/shard_map/cond
  120.3 5.2 %collective-permute-start.6 = (f32[1,1024]{1,0:T(1,128)S(1)}, f32[1,1024]{1,0:T(1,128)S(1)}, u32[]{:S(2)}, u32[]{:S(2)}) collective-permute-start(f32[1,1024]{1,0:T(1,128)S(1)} %bitcast.42), channel_id=1, source_target_pairs={{0,1},{1,0},{2,3},{3,2},{4,5},{5,4},{6,7},{7,6},{8,9},{9,8},{10,11... | collective-permute-start | bytes 12296 | tf_op jit(solution)/shard_map/cond/branch_1_fun/ppermute | solution.py:33
  122.0 4.1 %collective-permute-start.7 = (f32[1,256]{1,0:T(1,128)S(1)}, f32[1,256]{1,0:T(1,128)S(1)}, u32[]{:S(2)}, u32[]{:S(2)}) collective-permute-start(f32[1,256]{1,0:T(1,128)S(1)} %bitcast.46), channel_id=1, source_target_pairs={{0,1},{1,0},{2,3},{3,2},{4,5},{5,4},{6,7},{7,6},{8,9},{9,8},{10,11... | collective-permute-start | bytes 3080 | tf_op jit(solution)/shard_map/cond/branch_1_fun/ppermute | solution.py:33
  125.0 6.1 %collective-permute-start.9 = (bf16[64,1024]{1,0:T(8,128)(2,1)}, bf16[64,1024]{1,0:T(8,128)(2,1)S(1)}, u32[]{:S(2)}, u32[]{:S(2)}) collective-permute-start(bf16[64,1024]{1,0:T(8,128)(2,1)} %get-tuple-element.94), channel_id=1, source_target_pairs={{0,4},{2,6},{4,0},{6,2},{8,12},{10,14},{12,8},{14,10},{16,20},{18,... | collective-permute-start | bytes 393224 | tf_op jit(solution)/shard_map/cond/branch_1_fun/ppermute | solution.py:33
  126.1 5.0 %copy-start.37 = (f32[1,256]{1,0:T(1,128)}, f32[1,256]{1,0:T(1,128)S(1)}, u32[]{:S(2)}) copy-start(f32[1,256]{1,0:T(1,128)S(1)} %collective-permute-done.7.refs_2_) | copy-start | bytes 3076 | tf_op jit(solution)/shard_map/cond
  131.1 0.8 copy-start.3
  131.9 3.0 %copy-start.38 = (f32[1,256]{1,0:T(1,128)S(1)}, f32[1,256]{1,0:T(1,128)}, u32[]{:S(2)}) copy-start(f32[1,256]{1,0:T(1,128)} %copy-done.37) | copy-start | bytes 3076 | tf_op jit(solution)/shard_map/cond
  134.1 2.9 %collective-permute-start.10 = (bf16[512,1024]{1,0:T(8,128)(2,1)}, bf16[512,1024]{1,0:T(8,128)(2,1)S(1)}, u32[]{:S(2)}, u32[]{:S(2)}) collective-permute-start(bf16[512,1024]{1,0:T(8,128)(2,1)} %pad_maximum_fusion), channel_id=1, source_target_pairs={{0,2},{2,0},{4,6},{6,4},{8,10},{10,8},{12,14},{14,12},{16,18},{18,... | collective-permute-start | bytes 3145736 | tf_op jit(solution)/shard_map/cond/branch_1_fun/ppermute | solution.py:33
  136.9 1.0 copy-start.16
  137.9 3.6 %copy-start.13 = (bf16[256,1024]{1,0:T(8,128)(2,1)S(1)}, bf16[256,1024]{1,0:T(8,128)(2,1)}, u32[]{:S(2)}) copy-start(bf16[256,1024]{1,0:T(8,128)(2,1)} %get-tuple-element.102.refs_0_) | copy-start | bytes 1572868 | tf_op jit(solution)/shard_map/cond
  141.4 2.8 %copy-start.40 = (bf16[80,1024]{1,0:T(8,128)(2,1)S(1)}, bf16[80,1024]{1,0:T(8,128)(2,1)}, u32[]{:S(2)}) copy-start(bf16[80,1024]{1,0:T(8,128)(2,1)} %get-tuple-element.98) | copy-start | bytes 491524 | tf_op jit(solution)/shard_map/cond
  141.4 5.7 %copy-start.39 = (bf16[80,1024]{1,0:T(8,128)(2,1)S(1)}, bf16[80,1024]{1,0:T(8,128)(2,1)}, u32[]{:S(2)}) copy-start(bf16[80,1024]{1,0:T(8,128)(2,1)} %get-tuple-element.99) | copy-start | bytes 491524 | tf_op jit(solution)/shard_map/cond
  141.4 6.0 %copy-start.1 = (bf16[1024,1024]{1,0:T(8,128)(2,1)S(1)}, bf16[1024,1024]{1,0:T(8,128)(2,1)}, u32[]{:S(2)}) copy-start(bf16[1024,1024]{1,0:T(8,128)(2,1)} %get-tuple-element.103) | copy-start | bytes 6291460 | tf_op jit(solution)/shard_map/cond
  141.5 20.1 %copy-start.6 = (f32[80,1024]{1,0:T(8,128)S(1)}, f32[80,1024]{1,0:T(8,128)}, u32[]{:S(2)}) copy-start(f32[80,1024]{1,0:T(8,128)} %get-tuple-element.96.refs_1_) | copy-start | bytes 983044 | tf_op jit(solution)/shard_map/cond
  141.5 14.9 %collective-permute-start.11 = (bf16[80,1024]{1,0:T(8,128)(2,1)}, bf16[80,1024]{1,0:T(8,128)(2,1)S(1)}, u32[]{:S(2)}, u32[]{:S(2)}) collective-permute-start(bf16[80,1024]{1,0:T(8,128)(2,1)} %get-tuple-element.97), channel_id=1, source_target_pairs={{0,8},{2,10},{4,12},{6,14},{8,0},{10,2},{12,4},{14,6},{16,24},{18,... | collective-permute-start | bytes 491528 | tf_op jit(solution)/shard_map/cond/branch_1_fun/ppermute | solution.py:33
  144.2 12.2 %collective-permute-start.12 = (bf16[80,1024]{1,0:T(8,128)(2,1)S(1)}, bf16[80,1024]{1,0:T(8,128)(2,1)S(1)}, u32[]{:S(2)}, u32[]{:S(2)}) collective-permute-start(bf16[80,1024]{1,0:T(8,128)(2,1)S(1)} %copy-done.40), channel_id=1, source_target_pairs={{0,16},{2,18},{4,20},{6,22},{8,24},{10,26},{12,28},{14,30},{16,0},... | collective-permute-start | bytes 491528 | tf_op jit(solution)/shard_map/cond/branch_1_fun/ppermute | solution.py:33
  147.1 14.5 %collective-permute-start.13 = (bf16[80,1024]{1,0:T(8,128)(2,1)S(1)}, bf16[80,1024]{1,0:T(8,128)(2,1)S(1)}, u32[]{:S(2)}, u32[]{:S(2)}) collective-permute-start(bf16[80,1024]{1,0:T(8,128)(2,1)S(1)} %copy-done.39), channel_id=1, source_target_pairs={{0,24},{2,26},{4,28},{6,30},{8,16},{10,18},{12,20},{14,22},{16,8},... | collective-permute-start | bytes 491528 | tf_op jit(solution)/shard_map/cond/branch_1_fun/ppermute | solution.py:33
  148.1 18.9 %copy-start.14 = (f32[256,512]{1,0:T(8,128)S(1)}, f32[256,512]{1,0:T(8,128)}, u32[]{:S(2)}) copy-start(f32[256,512]{1,0:T(8,128)} %after.8) | copy-start | bytes 1572868 | tf_op jit(solution)/shard_map/cond
  161.7 11.2 %collective-permute-start.16 = (bf16[80,1024]{1,0:T(8,128)(2,1)S(1)}, bf16[80,1024]{1,0:T(8,128)(2,1)S(1)}, u32[]{:S(2)}, u32[]{:S(2)}) collective-permute-start(bf16[80,1024]{1,0:T(8,128)(2,1)S(1)} %pad_maximum_fusion.4), channel_id=1, source_target_pairs={{0,8},{2,10},{4,12},{6,14},{8,0},{10,2},{12,4},{14,6},{16,24},{18,... | collective-permute-start | bytes 491528 | tf_op jit(solution)/shard_map/cond/branch_1_fun/ppermute | solution.py:33
  165.5 24.7 %copy-start.5 = (f32[256,1024]{1,0:T(8,128)S(1)}, f32[256,1024]{1,0:T(8,128)}, u32[]{:S(2)}) copy-start(f32[256,1024]{1,0:T(8,128)} %copy-done.4) | copy-start | bytes 3145732 | tf_op jit(solution)/shard_map/cond
  165.5 24.7 %copy-start.12 = (bf16[256,512]{1,0:T(8,128)(2,1)S(1)}, bf16[256,512]{1,0:T(8,128)(2,1)}, u32[]{:S(2)}) copy-start(bf16[256,512]{1,0:T(8,128)(2,1)} %get-tuple-element.100) | copy-start | bytes 786436 | tf_op jit(solution)/shard_map/cond
  165.5 24.6 %copy-start.18 = (bf16[256,512]{1,0:T(8,128)(2,1)S(1)}, bf16[256,512]{1,0:T(8,128)(2,1)}, u32[]{:S(2)}) copy-start(bf16[256,512]{1,0:T(8,128)(2,1)} %get-tuple-element.104) | copy-start | bytes 786436 | tf_op jit(solution)/shard_map/cond
  165.6 21.8 %collective-permute-start.17 = (f32[256,512]{1,0:T(8,128)S(1)}, f32[256,512]{1,0:T(8,128)S(1)}, u32[]{:S(2)}, u32[]{:S(2)}) collective-permute-start(f32[256,512]{1,0:T(8,128)S(1)} %slice_select_fusion.1), channel_id=1, source_target_pairs={{0,1},{1,0},{2,3},{3,2},{4,5},{5,4},{6,7},{7,6},{8,9},{9,8},{10,11... | collective-permute-start | bytes 1572872 | tf_op jit(solution)/shard_map/cond/branch_1_fun/ppermute | solution.py:33
  167.0 23.1 %collective-permute-start.18 = (f32[256,512]{1,0:T(8,128)S(1)}, f32[256,512]{1,0:T(8,128)S(1)}, u32[]{:S(2)}, u32[]{:S(2)}) collective-permute-start(f32[256,512]{1,0:T(8,128)S(1)} %copy-done.14), channel_id=1, source_target_pairs={{0,1},{1,0},{2,3},{3,2},{4,5},{5,4},{6,7},{7,6},{8,9},{9,8},{10,11... | collective-permute-start | bytes 1572872 | tf_op jit(solution)/shard_map/cond/branch_1_fun/ppermute | solution.py:33
  167.6 16.8 %collective-permute-start.15 = (bf16[80,1024]{1,0:T(8,128)(2,1)S(1)}, bf16[80,1024]{1,0:T(8,128)(2,1)S(1)}, u32[]{:S(2)}, u32[]{:S(2)}) collective-permute-start(bf16[80,1024]{1,0:T(8,128)(2,1)S(1)} %pad_maximum_fusion.4), channel_id=1, source_target_pairs={{0,16},{2,18},{4,20},{6,22},{8,24},{10,26},{12,28},{14,30},{16,0},... | collective-permute-start | bytes 491528 | tf_op jit(solution)/shard_map/cond/branch_1_fun/ppermute | solution.py:33
  168.5 18.6 %collective-permute-start.14 = (bf16[80,1024]{1,0:T(8,128)(2,1)S(1)}, bf16[80,1024]{1,0:T(8,128)(2,1)S(1)}, u32[]{:S(2)}, u32[]{:S(2)}) collective-permute-start(bf16[80,1024]{1,0:T(8,128)(2,1)S(1)} %pad_maximum_fusion.4), channel_id=1, source_target_pairs={{0,24},{2,26},{4,28},{6,30},{8,16},{10,18},{12,20},{14,22},{16,8},... | collective-permute-start | bytes 491528 | tf_op jit(solution)/shard_map/cond/branch_1_fun/ppermute | solution.py:33
  191.2 17.5 %collective-permute-start.28 = (bf16[320,1024]{1,0:T(8,128)(2,1)S(1)}, bf16[320,1024]{1,0:T(8,128)(2,1)S(1)}, u32[]{:S(2)}, u32[]{:S(2)}) collective-permute-start(bf16[320,1024]{1,0:T(8,128)(2,1)S(1)} %get-tuple-element.174.first_ref.rest_0_), channel_id=1, source_target_pairs={{0,4},{2,6},{4,0},{6,2},{8,12},{10,14},{12,8},{14,10},{16,20},{18,... | collective-permute-start | bytes 1966088 | tf_op jit(solution)/shard_map/ppermute | solution.py:33
  192.3 16.5 %collective-permute-start.30 = (bf16[320,1024]{1,0:T(8,128)(2,1)S(1)}, bf16[320,1024]{1,0:T(8,128)(2,1)S(1)}, u32[]{:S(2)}, u32[]{:S(2)}) collective-permute-start(bf16[320,1024]{1,0:T(8,128)(2,1)S(1)} %get-tuple-element.174.first_ref.rest_0_), channel_id=1, source_target_pairs={{0,2},{2,0},{4,6},{6,4},{8,10},{10,8},{12,14},{14,12},{16,18},{18,... | collective-permute-start | bytes 1966088 | tf_op jit(solution)/shard_map/ppermute | solution.py:33
  208.8 7.3 %copy-start.7 = (bf16[320,1024]{1,0:T(8,128)(2,1)}, bf16[320,1024]{1,0:T(8,128)(2,1)S(1)}, u32[]{:S(2)}) copy-start(bf16[320,1024]{1,0:T(8,128)(2,1)S(1)} %collective-permute-done.28.first_ref.rest_2_) | copy-start | bytes 1966084
  208.8 7.3 %collective-permute-start.29 = (bf16[320,1024]{1,0:T(8,128)(2,1)S(1)}, bf16[320,1024]{1,0:T(8,128)(2,1)S(1)}, u32[]{:S(2)}, u32[]{:S(2)}) collective-permute-start(bf16[320,1024]{1,0:T(8,128)(2,1)S(1)} %collective-permute-done.28.first_ref.rest_2_), channel_id=1, source_target_pairs={{0,2},{2,0},{4,6},{6,4},{8,10},{10,8},{12,14},{14,12},{16,18},{18,... | collective-permute-start | bytes 1966088 | tf_op jit(solution)/shard_map/ppermute | solution.py:33
  208.8 1.8 copy-start.9
  216.1 0.8 copy-start.8
  (9 other events, 6.0 us)
Sparse Core Ops, SparseCore 0:
  72.3 138.2 all-reduce.2

commit v25 on v19

--- a/solution.py
+++ b/solution.py
@@ -1315,10 +1315,10 @@
             [],
         )
         normed_mine, normed_other = narrow_halves(normed_part)
-        normed_theirs = swapped(after(normed_other, keep), "narrow", 1)
+        normed_theirs = swapped(after(normed_other.astype(bf16), keep), "narrow", 1).astype(f32)
         out_part = jnp.dot(after(gated, keep), out_weight, preferred_element_type=f32)
         out_mine, out_other = narrow_halves(out_part)
-        out_theirs = swapped(out_other, "narrow", 1)
+        out_theirs = swapped(out_other.astype(bf16), "narrow", 1).astype(f32)
         layer_out = (tokens.astype(f32) + (out_mine + out_theirs)).astype(bf16)
         row_sum = (row_part + row_theirs).reshape(rows, 1)
         gain_mine = jnp.where(right_half, norm_gain[features:], norm_gain[:features])

time: 228 us -> 230 us (level)
    psum x1, waiting for transfers between devices: 0.42 us -> 5.05 us  [local(): out_sum, gate_sum = lax.psum(products, 'wide')]
    ppermute x26, waiting for transfers between devices: 62.7 us -> 60.3 us  [swapped(): return lax.ppermute(array, axis, [(i, i ^ bit) for i in range(peers)])]
  transfers between devices with their start and end apart: 32 -> 32, of which waited for: 15 -> 14; matrix products, arithmetic and copies ran while one was open for 8% -> 8% of each run, Pallas kernels for 26% -> 26%
where the time goes in v25:
time: 230 us; the launch traced here: 229 us
  Pallas kernels  78.8 us (34%)
  waiting for transfers between devices  67.1 us (29%)
  starting transfers between devices  45.9 us (20%)
  between operations  14.3 us (6%)
  matrix products  9.63 us (4%)
  other arithmetic  7.52 us (3%)
  local copies, waits for them, and re-layouts  5.48 us (2%)
    ppermute x26, waiting for transfers between devices, swapped(): return lax.ppermute(array, axis, [(i, i ^ bit) for i in range(peers)])  60.3 us
    pallas_call x5, Pallas kernels, call(): pl.pallas_call(kernel, grid=(width // scan_width,), in_specs=in_specs, ou...  52 us
    ppermute x26, starting transfers between devices, swapped(): return lax.ppermute(array, axis, [(i, i ^ bit) for i in range(peers)])  32.8 us
    ppermute x4, starting transfers between devices, passed_along(): return lax.ppermute(array, axis, pairs)  11.7 us
    pallas_call x2, Pallas kernels, joined(): pl.pallas_call(kernel, grid_spec=pltpu.PrefetchScalarGridSpec(num_scalar_...  10.5 us
    psum x1, waiting for transfers between devices, local(): out_sum, gate_sum = lax.psum(products, 'wide')  5.05 us
  transfers between devices with their start and end apart: 32, of which 14 were waited for; matrix products, arithmetic and copies ran while one was open for 8% of the time, Pallas kernels for 26%

profile of v25, /device:TPU:0, one launch (start us, length us, event | category | flops | bytes accessed | tf_op | source)
XLA Modules:
  0.0 229.0 jit_solution(2997887468530703648)
XLA Ops:
  7.2 3.0 %collective-permute-start.19 = (bf16[256,512]{1,0:T(8,128)(2,1)}, bf16[256,512]{1,0:T(8,128)(2,1)S(1)}, u32[]{:S(2)}, u32[]{:S(2)}) collective-permute-start(bf16[256,512]{1,0:T(8,128)(2,1)} %own_ref.1), channel_id=1, source_target_pairs={{0,1},{1,0},{2,3},{3,2},{4,5},{5,4},{6,7},{7,6},{8,9},{9,8},{10,11... | collective-permute-start | bytes 786440 | tf_op jit(solution)/shard_map/ppermute | solution.py:33
  10.3 1.4 edge_rows.1
  11.6 1.3 collective-permute-start.21
  13.0 4.0 %collective-permute-start.20 = (bf16[16,512]{1,0:T(8,128)(2,1)}, bf16[16,512]{1,0:T(8,128)(2,1)S(1)}, u32[]{:S(2)}, u32[]{:S(2)}) collective-permute-start(bf16[16,512]{1,0:T(8,128)(2,1)} %edge_rows.1), channel_id=1, source_target_pairs={{0,2},{2,4},{4,6},{6,8},{8,10},{10,12},{12,14},{14,16},{16,18},{18... | collective-permute-start | bytes 49160 | tf_op jit(solution)/shard_map/ppermute | solution.py:28
  17.0 1.6 collective-permute-start.23
  19.3 2.3 normalized.1
  21.6 4.0 %fusion.25.inner_ref.gate_ref = bf16[2,272,1024]{2,1,0:T(8,128)(2,1)S(1)} fusion(bf16[1024,2,1024]{2,1,0:T(2,128)(2,1)} %param.17, bf16[272,1024]{1,0:T(8,128)(2,1)} %get-tuple-element.152), kind=kOutput, calls=%fused_computation.47 | convolution fusion | flops 1141407744 | bytes 5865472 | tf_op jit(solution)/shard_map/td,dce->cte/dot_general | solution.py:1212
  25.6 3.1 %convolve.1 = (f32[256,1024]{1,0:T(8,128)}, bf16[256,1024]{1,0:T(8,128)(2,1)S(1)}, f32[96,256]{1,0:T(8,128)S(1)}) custom-call(bf16[2,272,1024]{2,1,0:T(8,128)(2,1)S(1)} %fusion.25.inner_ref.gate_ref, f32[4,1024]{1,0:T(4,128)S(1)} %copy-done.28, f32[1,1024]{1,0:T(1,128)} %bitcast.40, bf16[96,1024]{1,0:T(8,128)(2,1)S(1)} %copy-done.19, ...), custom_call_target="tpu_custom_call" | custom-call | flops 1 | bytes 1 | tf_op jit(solution)/shard_map/convolve/pallas_call | solution.py:127
  28.7 0.9 collective-permute-start.22
  29.8 0.7 fusion.29.gated_grad_ref
  30.5 2.8 %collective-permute-done.22.other_ref = f32[96,256]{1,0:T(8,128)S(1)} collective-permute-done((f32[96,256]{1,0:T(8,128)S(1)}, f32[96,256]{1,0:T(8,128)S(1)}, u32[]{:S(2)}, u32[]{:S(2)}) %collective-permute-start.22) | collective-permute-done | bytes 98336 | tf_op jit(solution)/shard_map/ppermute | solution.py:33
  33.4 10.0 %scan_ends.1 = (f32[256,1024]{1,0:T(8,128)}, f32[256,1024]{1,0:T(8,128)}, bf16[48,1024]{1,0:T(8,128)(2,1)}) custom-call(f32[96,256]{1,0:T(8,128)S(1)} %get-tuple-element.154.selected_ref, f32[96,256]{1,0:T(8,128)S(1)} %collective-permute-done.22.other_ref, bf16[64,1024]{1,0:T(8,128)(2,1)S(1)} %copy-done.20, f32[1,1024]{1,0:T(1,128)} %bitcast.41, ...), custom_call_target="tpu_custom_call" | custom-call | flops 1 | bytes 1 | tf_op jit(solution)/shard_map/scan_ends/pallas_call | solution.py:127
  43.5 1.6 collective-permute-done.24.other_ref
  45.1 1.7 carry_round.2
  46.8 1.7 collective-permute-start.25
  48.5 3.5 %collective-permute-done.25.other_ref = bf16[48,1024]{1,0:T(8,128)(2,1)} collective-permute-done((bf16[48,1024]{1,0:T(8,128)(2,1)}, bf16[48,1024]{1,0:T(8,128)(2,1)}, u32[]{:S(2)}, u32[]{:S(2)}) %collective-permute-start.25) | collective-permute-done | bytes 98336 | tf_op jit(solution)/shard_map/ppermute | solution.py:33
  52.0 1.8 carry_round.3
  53.7 4.6 %collective-permute-start.26 = (bf16[16,1024]{1,0:T(8,128)(2,1)}, bf16[16,1024]{1,0:T(8,128)(2,1)S(1)}, u32[]{:S(2)}, u32[]{:S(2)}) collective-permute-start(bf16[16,1024]{1,0:T(8,128)(2,1)} %get-tuple-element.162), channel_id=1, source_target_pairs={{0,8},{2,10},{4,12},{6,14},{8,16},{10,18},{12,20},{14,22},{16,24},... | collective-permute-start | bytes 98312 | tf_op jit(solution)/shard_map/ppermute | solution.py:28
  58.3 1.5 collective-permute-start.27
  59.8 1.9 pad_maximum_fusion.5.cot_ref
  61.7 0.6 copy-done.29
  62.4 11.3 %scan_forward.1 = (bf16[256,1024]{1,0:T(8,128)(2,1)}, bf16[256,1024]{1,0:T(8,128)(2,1)}, bf16[1024,1024]{1,0:T(8,128)(2,1)}, bf16[1024,1024]{1,0:T(8,128)(2,1)}, f32[16,1024]{1,0:T(8,128)}) custom-call(f32[96,256]{1,0:T(8,128)S(1)} %get-tuple-element.154.selected_ref, f32[96,256]{1,0:T(8,128)} %copy-done.18, f32[256,1024]{1,0:T(8,128)} %get-tuple-element.157.step_ref, ...), custom_call_target="tpu_custom_call" | custom-call | flops 1 | bytes 1 | tf_op jit(solution)/shard_map/scan_forward/pallas_call | solution.py:127
  73.7 114.9 %conditional.1 = (bf16[320,1024]{1,0:T(8,128)(2,1)S(1)}, bf16[256,512]{1,0:T(8,128)(2,1)}, bf16[256,512]{1,0:T(8,128)(2,1)}) conditional(s32[]{:T(128)} %convert_element_type.55, () %tuple.16, (s32[]{:T(128)}, f32[1024]{0:T(1024)}, f32[96,256]{1,0:T(8,128)S(1)}, f32[96,256]{1,0:T(8,128)}, f32[256,1024]{1,0:T(8,128)}, ...), branch_computations={%region_0.1_spmd, %region_1.4_spmd} | conditional | flops 1622038784 | bytes 78968648 | solution.py:1343
  73.7 23.5 %scan_backward.1 = (f32[256,1024]{1,0:T(8,128)}, f32[96,256]{1,0:T(8,128)}, f32[82,1024]{1,0:T(8,128)}) custom-call(f32[96,256]{1,0:T(8,128)S(1)} %get-tuple-element.62.selected_ref, f32[96,256]{1,0:T(8,128)} %get-tuple-element.63.other_ref, f32[256,1024]{1,0:T(8,128)} %get-tuple-element.64.step_pre_ref, f32[256,1024]{1,0:T(8,128)} %get-tuple-element.65.step_ref, ...), custom_call_target="tpu_custom_call" | custom-call | flops 1 | bytes 1 | tf_op jit(solution)/shard_map/cond/branch_1_fun/scan_backward/pallas_call | solution.py:127
  97.2 1.5 collective-permute-start
  98.7 0.8 constant_dynamic-slice_fusion
  99.6 0.7 collective-permute-start.3
  100.3 1.4 collective-permute-start.2
  102.2 4.1 %convolve_grad.1 = (bf16[256,1024]{1,0:T(8,128)(2,1)}, f32[8,1024]{1,0:T(8,128)}, f32[8,1024]{1,0:T(8,128)}, f32[101,1024]{1,0:T(8,128)}) custom-call(f32[96,256]{1,0:T(8,128)} %get-tuple-element.76.select_grad_ref.refs_1_, f32[96,256]{1,0:T(8,128)} %collective-permute-done.other_ref, bf16[96,1024]{1,0:T(8,128)(2,1)} %get-tuple-element.77.select_ref, ...), custom_call_target="tpu_custom_call" | custom-call | flops 1 | bytes 1 | tf_op jit(solution)/shard_map/cond/branch_1_fun/convolve_grad/pallas_call | solution.py:127
  106.3 1.6 collective-permute-start.1
  108.0 1.7 collective-permute-done.1.next_ref
  110.5 1.4 patched.1.wait_ref.own_ref
  112.0 1.4 collective-permute-start.5
  113.3 2.2 small_halves.1
  115.5 3.1 %collective-permute-start.8 = (bf16[128,1024]{1,0:T(8,128)(2,1)}, bf16[128,1024]{1,0:T(8,128)(2,1)S(1)}, u32[]{:S(2)}, u32[]{:S(2)}) collective-permute-start(bf16[128,1024]{1,0:T(8,128)(2,1)} %get-tuple-element.93), channel_id=1, source_target_pairs={{0,2},{2,0},{4,6},{6,4},{8,10},{10,8},{12,14},{14,12},{16,18},{18,... | collective-permute-start | bytes 786440 | tf_op jit(solution)/shard_map/cond/branch_1_fun/ppermute | solution.py:33
  118.6 4.2 %fusion.7 = (f32[256]{0:T(256)S(1)}, f32[1024]{0:T(1024)S(1)}, f32[256,1024]{1,0:T(8,128)S(1)}) fusion(bf16[256,1024]{1,0:T(8,128)(2,1)S(1)} %copy-done.38, f32[1024]{0:T(1024)S(1)} %copy-done.31, f32[256]{0:T(256)S(1)} %bitcast.37, bf16[1024,2,1024]{2,1,0:T(2,128)(2,1)} %get-tuple-element.208, bf16[1,256,1024]{2,1,0:T(8,128)(2,1)S(1)} %bitcast.48, ...), kind=kOutput, calls=%fused_computation.7 | convolution fusion | flops 1076099840 | bytes 6825984 | tf_op jit(solution)/shard_map/cond/branch_1_fun/cte,dce->td/dot_general | solution.py:1296
  122.9 1.5 collective-permute-start.6
  125.0 0.7 copy-done.26
  125.7 1.9 folded.1
  128.4 5.3 %collective-permute-done.9.refs_3_.arrived_ref = bf16[64,1024]{1,0:T(8,128)(2,1)S(1)} collective-permute-done((bf16[64,1024]{1,0:T(8,128)(2,1)}, bf16[64,1024]{1,0:T(8,128)(2,1)S(1)}, u32[]{:S(2)}, u32[]{:S(2)}) %collective-permute-start.9) | collective-permute-done | bytes 131104 | tf_op jit(solution)/shard_map/cond/branch_1_fun/ppermute | solution.py:33
  133.7 0.6 copy-done.24
  134.5 2.1 pad_maximum_fusion
  137.2 0.8 select_convert_fusion.refs_0_
  138.0 1.7 collective-permute-done.10.far_ref
  139.6 3.7 %inner_quarter.1 = (f32[80,1024]{1,0:T(8,128)}, bf16[80,1024]{1,0:T(8,128)(2,1)}, bf16[80,1024]{1,0:T(8,128)(2,1)}, bf16[80,1024]{1,0:T(8,128)(2,1)}) custom-call(s32[1]{0:T(128)} %bitcast.place_ref, bf16[256,1024]{1,0:T(8,128)(2,1)} %patched.1.wait_ref.own_ref, bf16[256,1024]{1,0:T(8,128)(2,1)} %after.6.near_ref, ...), custom_call_target="tpu_custom_call" | custom-call | flops 1 | bytes 1 | tf_op jit(solution)/shard_map/cond/branch_1_fun/inner_quarter/pallas_call | solution.py:1000
  143.3 2.9 %collective-permute-start.11 = (bf16[80,1024]{1,0:T(8,128)(2,1)}, bf16[80,1024]{1,0:T(8,128)(2,1)S(1)}, u32[]{:S(2)}, u32[]{:S(2)}) collective-permute-start(bf16[80,1024]{1,0:T(8,128)(2,1)} %get-tuple-element.97), channel_id=1, source_target_pairs={{0,8},{2,10},{4,12},{6,14},{8,0},{10,2},{12,4},{14,6},{16,24},{18,... | collective-permute-start | bytes 491528 | tf_op jit(solution)/shard_map/cond/branch_1_fun/ppermute | solution.py:33
  146.2 2.9 %collective-permute-start.12 = (bf16[80,1024]{1,0:T(8,128)(2,1)}, bf16[80,1024]{1,0:T(8,128)(2,1)S(1)}, u32[]{:S(2)}, u32[]{:S(2)}) collective-permute-start(bf16[80,1024]{1,0:T(8,128)(2,1)} %get-tuple-element.98), channel_id=1, source_target_pairs={{0,16},{2,18},{4,20},{6,22},{8,24},{10,26},{12,28},{14,30},{16,0},... | collective-permute-start | bytes 491528 | tf_op jit(solution)/shard_map/cond/branch_1_fun/ppermute | solution.py:33
  149.3 1.3 collective-permute-start.18
  150.6 0.7 fusion.30
  151.4 0.8 collective-permute-start.17
  152.2 5.7 %collective-permute-done.11 = bf16[80,1024]{1,0:T(8,128)(2,1)S(1)} collective-permute-done((bf16[80,1024]{1,0:T(8,128)(2,1)}, bf16[80,1024]{1,0:T(8,128)(2,1)S(1)}, u32[]{:S(2)}, u32[]{:S(2)}) %collective-permute-start.11) | collective-permute-done | bytes 163872 | tf_op jit(solution)/shard_map/cond/branch_1_fun/ppermute | solution.py:33
  157.9 5.3 %collective-permute-done.12 = bf16[80,1024]{1,0:T(8,128)(2,1)S(1)} collective-permute-done((bf16[80,1024]{1,0:T(8,128)(2,1)}, bf16[80,1024]{1,0:T(8,128)(2,1)S(1)}, u32[]{:S(2)}, u32[]{:S(2)}) %collective-permute-start.12) | collective-permute-done | bytes 163872 | tf_op jit(solution)/shard_map/cond/branch_1_fun/ppermute | solution.py:33
  163.4 3.7 %collective-permute-start.16 = (bf16[80,1024]{1,0:T(8,128)(2,1)S(1)}, bf16[80,1024]{1,0:T(8,128)(2,1)S(1)}, u32[]{:S(2)}, u32[]{:S(2)}) collective-permute-start(bf16[80,1024]{1,0:T(8,128)(2,1)S(1)} %pad_maximum_fusion.4), channel_id=1, source_target_pairs={{0,8},{2,10},{4,12},{6,14},{8,0},{10,2},{12,4},{14,6},{16,24},{18,... | collective-permute-start | bytes 491528 | tf_op jit(solution)/shard_map/cond/branch_1_fun/ppermute | solution.py:33
  167.7 1.9 collective-permute-start.14
  169.6 1.0 fusion.15
  170.6 4.9 %collective-permute-done.16 = bf16[80,1024]{1,0:T(8,128)(2,1)S(1)} collective-permute-done((bf16[80,1024]{1,0:T(8,128)(2,1)S(1)}, bf16[80,1024]{1,0:T(8,128)(2,1)S(1)}, u32[]{:S(2)}, u32[]{:S(2)}) %collective-permute-start.16) | collective-permute-done | bytes 163872 | tf_op jit(solution)/shard_map/cond/branch_1_fun/ppermute | solution.py:33
  175.6 8.4 %collective-permute-done.15 = bf16[80,1024]{1,0:T(8,128)(2,1)S(1)} collective-permute-done((bf16[80,1024]{1,0:T(8,128)(2,1)S(1)}, bf16[80,1024]{1,0:T(8,128)(2,1)S(1)}, u32[]{:S(2)}, u32[]{:S(2)}) %collective-permute-start.15) | collective-permute-done | bytes 163872 | tf_op jit(solution)/shard_map/cond/branch_1_fun/ppermute | solution.py:33
  183.9 4.4 %collective-permute-done.14 = bf16[80,1024]{1,0:T(8,128)(2,1)S(1)} collective-permute-done((bf16[80,1024]{1,0:T(8,128)(2,1)S(1)}, bf16[80,1024]{1,0:T(8,128)(2,1)S(1)}, u32[]{:S(2)}, u32[]{:S(2)}) %collective-permute-start.14) | collective-permute-done | bytes 163872 | tf_op jit(solution)/shard_map/cond/branch_1_fun/ppermute | solution.py:33
  188.6 0.9 collective-permute-start.28
  189.5 16.2 %collective-permute-done.28.first_ref.rest_2_ = bf16[320,1024]{1,0:T(8,128)(2,1)S(1)} collective-permute-done((bf16[320,1024]{1,0:T(8,128)(2,1)S(1)}, bf16[320,1024]{1,0:T(8,128)(2,1)S(1)}, u32[]{:S(2)}, u32[]{:S(2)}) %collective-permute-start.28) | collective-permute-done | bytes 655392 | tf_op jit(solution)/shard_map/ppermute | solution.py:33
  205.7 5.1 %all-reduce.3.cloned.1.call-done = (bf16[1024,1024]{1,0:T(8,128)(2,1)}, bf16[1024,1024]{1,0:T(8,128)(2,1)}) async-done(((bf16[1024,1024]{1,0:T(8,128)(2,1)}, bf16[1024,1024]{1,0:T(8,128)(2,1)}), (bf16[1024,1024]{1,0:T(8,128)(2,1)}, bf16[1024,1024]{1,0:T(8,128)(2,1)})) %all-reduce.3.cloned.1.call-update) | async-done | bytes 4194320 | tf_op jit(solution)/shard_map/psum | solution.py:1251
  210.8 5.4 %joined.2 = (f32[1024,2,1024]{2,1,0:T(2,128)}, f32[1024,1024]{1,0:T(8,128)}) custom-call(s32[1]{0:T(128)} %bitcast.21.place_ref, bf16[1024,1024]{1,0:T(8,128)(2,1)} %get-tuple-element.219.gate_ref, bf16[320,1024]{1,0:T(8,128)(2,1)S(1)} %get-tuple-element.174.first_ref.rest_0_, bf16[320,1024]{1,0:T(8,128)(2,1)} %copy-done.7, ...), custom_call_target="tpu_custom_call" | custom-call | flops 1 | bytes 1 | tf_op jit(solution)/shard_map/joined/pallas_call | solution.py:1070
  216.2 0.8 copy-done.6
  217.1 5.0 %joined.3 = (f32[1024,2,1024]{2,1,0:T(2,128)}, f32[64,1024]{1,0:T(8,128)}, f32[16,1024]{1,0:T(8,128)}, f32[1,1024]{1,0:T(1,128)}, f32[1,1024]{1,0:T(1,128)}, /*i...) custom-call(s32[1]{0:T(128)} %bitcast.21.place_ref, ...), custom_call_target="tpu_custom_call", output_to_operand_aliasing={{0}: (8, {})} | custom-call | flops 1 | bytes 1 | tf_op jit(solution)/shard_map/joined/pallas_call | solution.py:1070
  (127 shorter events, 5.9 us)
Async XLA Ops:
  7.2 203.6 %all-reduce.3.cloned.1.call-start = ((), (), s32[]{:S(2)}) async-start(), calls=%async_computation | async-start | bytes 8388608 | tf_op jit(solution)/shard_map/psum | solution.py:1251
  7.2 11.4 %collective-permute-start.19 = (bf16[256,512]{1,0:T(8,128)(2,1)}, bf16[256,512]{1,0:T(8,128)(2,1)S(1)}, u32[]{:S(2)}, u32[]{:S(2)}) collective-permute-start(bf16[256,512]{1,0:T(8,128)(2,1)} %own_ref.1), channel_id=1, source_target_pairs={{0,1},{1,0},{2,3},{3,2},{4,5},{5,4},{6,7},{7,6},{8,9},{9,8},{10,11... | collective-permute-start | bytes 786440 | tf_op jit(solution)/shard_map/ppermute | solution.py:33
  11.6 7.0 %collective-permute-start.21 = (bf16[16,512]{1,0:T(8,128)(2,1)}, bf16[16,512]{1,0:T(8,128)(2,1)S(1)}, u32[]{:S(2)}, u32[]{:S(2)}) collective-permute-start(bf16[16,512]{1,0:T(8,128)(2,1)} %edge_rows.1), channel_id=1, source_target_pairs={{0,3},{1,2},{2,5},{3,4},{4,7},{5,6},{6,9},{7,8},{8,11},{9,10},{10,... | collective-permute-start | bytes 49160 | tf_op jit(solution)/shard_map/ppermute | solution.py:51
  13.0 5.6 %collective-permute-start.20 = (bf16[16,512]{1,0:T(8,128)(2,1)}, bf16[16,512]{1,0:T(8,128)(2,1)S(1)}, u32[]{:S(2)}, u32[]{:S(2)}) collective-permute-start(bf16[16,512]{1,0:T(8,128)(2,1)} %edge_rows.1), channel_id=1, source_target_pairs={{0,2},{2,4},{4,6},{6,8},{8,10},{10,12},{12,14},{14,16},{16,18},{18... | collective-permute-start | bytes 49160 | tf_op jit(solution)/shard_map/ppermute | solution.py:28
  17.0 12.7 %collective-permute-start.23 = (bf16[256,512]{1,0:T(8,128)(2,1)}, bf16[256,512]{1,0:T(8,128)(2,1)S(1)}, u32[]{:S(2)}, u32[]{:S(2)}) collective-permute-start(bf16[256,512]{1,0:T(8,128)(2,1)} %param.27), channel_id=1, source_target_pairs={{0,1},{1,0},{2,3},{3,2},{4,5},{5,4},{6,7},{7,6},{8,9},{9,8},{10,11... | collective-permute-start | bytes 786440 | tf_op jit(solution)/shard_map/ppermute | solution.py:33
  21.6 4.0 %copy-start.19 = (bf16[96,1024]{1,0:T(8,128)(2,1)S(1)}, bf16[96,1024]{1,0:T(8,128)(2,1)}, u32[]{:S(2)}) copy-start(bf16[96,1024]{1,0:T(8,128)(2,1)} %select_ref.1) | copy-start | bytes 589828
  21.6 4.0 %copy-start.28 = (f32[4,1024]{1,0:T(4,128)S(1)}, f32[4,1024]{1,0:T(4,128)}, u32[]{:S(2)}) copy-start(f32[4,1024]{1,0:T(4,128)} %conv_weight_ref.1) | copy-start | bytes 49156
  21.6 8.1 %copy-start.15 = (bf16[256,512]{1,0:T(8,128)(2,1)S(1)}, bf16[256,512]{1,0:T(8,128)(2,1)}, u32[]{:S(2)}) copy-start(bf16[256,512]{1,0:T(8,128)(2,1)} %param.27) | copy-start | bytes 786436
  25.6 4.2 %copy-start = (bf16[1024,1024]{1,0:T(8,128)(2,1)S(1)}, bf16[1024,1024]{1,0:T(8,128)(2,1)}, u32[]{:S(2)}) copy-start(bf16[1024,1024]{1,0:T(8,128)(2,1)} %param.25) | copy-start | bytes 6291460
  28.7 4.6 %collective-permute-start.22 = (f32[96,256]{1,0:T(8,128)S(1)}, f32[96,256]{1,0:T(8,128)S(1)}, u32[]{:S(2)}, u32[]{:S(2)}) collective-permute-start(f32[96,256]{1,0:T(8,128)S(1)} %get-tuple-element.154.selected_ref), channel_id=1, source_target_pairs={{0,1},{1,0},{2,3},{3,2},{4,5},{5,4},{6,7},{7,6},{8,9},{9,8},{10,11... | collective-permute-start | bytes 294920 | tf_op jit(solution)/shard_map/ppermute | solution.py:33
  29.7 13.6 %copy-start.9 = (bf16[256,512]{1,0:T(8,128)(2,1)}, bf16[256,512]{1,0:T(8,128)(2,1)S(1)}, u32[]{:S(2)}) copy-start(bf16[256,512]{1,0:T(8,128)(2,1)S(1)} %get-tuple-element.236) | copy-start | bytes 786436
  29.7 13.6 %copy-start.10 = (bf16[256,512]{1,0:T(8,128)(2,1)}, bf16[256,512]{1,0:T(8,128)(2,1)S(1)}, u32[]{:S(2)}) copy-start(bf16[256,512]{1,0:T(8,128)(2,1)S(1)} %get-tuple-element.237) | copy-start | bytes 786436
  29.7 3.6 %copy-start.14 = (f32[16,1024]{1,0:T(8,128)S(1)}, f32[16,1024]{1,0:T(8,128)}, u32[]{:S(2)}) copy-start(f32[16,1024]{1,0:T(8,128)} %decay_log_ref.7) | copy-start | bytes 196612
  29.8 3.6 %copy-start.20 = (bf16[64,1024]{1,0:T(8,128)(2,1)S(1)}, bf16[64,1024]{1,0:T(8,128)(2,1)}, u32[]{:S(2)}) copy-start(bf16[64,1024]{1,0:T(8,128)(2,1)} %step_weight_ref.1) | copy-start | bytes 393220
  33.4 10.0 %copy-start.18 = (f32[96,256]{1,0:T(8,128)}, f32[96,256]{1,0:T(8,128)S(1)}, u32[]{:S(2)}) copy-start(f32[96,256]{1,0:T(8,128)S(1)} %collective-permute-done.22.other_ref) | copy-start | bytes 294916
  43.4 1.7 collective-permute-start.24
  46.8 5.2 %collective-permute-start.25 = (bf16[48,1024]{1,0:T(8,128)(2,1)}, bf16[48,1024]{1,0:T(8,128)(2,1)}, u32[]{:S(2)}, u32[]{:S(2)}) collective-permute-start(bf16[48,1024]{1,0:T(8,128)(2,1)} %get-tuple-element.159.own_ref), channel_id=1, source_target_pairs={{0,4},{2,6},{4,0},{6,2},{8,12},{10,14},{12,8},{14,10},{16,20},{18,... | collective-permute-start | bytes 294920 | tf_op jit(solution)/shard_map/ppermute | solution.py:33
  53.7 8.0 %collective-permute-start.26 = (bf16[16,1024]{1,0:T(8,128)(2,1)}, bf16[16,1024]{1,0:T(8,128)(2,1)S(1)}, u32[]{:S(2)}, u32[]{:S(2)}) collective-permute-start(bf16[16,1024]{1,0:T(8,128)(2,1)} %get-tuple-element.162), channel_id=1, source_target_pairs={{0,8},{2,10},{4,12},{6,14},{8,16},{10,18},{12,20},{14,22},{16,24},... | collective-permute-start | bytes 98312 | tf_op jit(solution)/shard_map/ppermute | solution.py:28
  58.3 15.3 %collective-permute-start.27 = (bf16[16,1024]{1,0:T(8,128)(2,1)}, bf16[16,1024]{1,0:T(8,128)(2,1)S(1)}, u32[]{:S(2)}, u32[]{:S(2)}) collective-permute-start(bf16[16,1024]{1,0:T(8,128)(2,1)} %get-tuple-element.165), channel_id=1, source_target_pairs={{8,0},{10,2},{12,4},{14,6},{16,8},{18,10},{20,12},{22,14},{24,16},... | collective-permute-start | bytes 98312 | tf_op jit(solution)/shard_map/ppermute | solution.py:28
  97.2 5.0 %copy-start.17 = (f32[256,1024]{1,0:T(8,128)S(1)}, f32[256,1024]{1,0:T(8,128)}, u32[]{:S(2)}) copy-start(f32[256,1024]{1,0:T(8,128)} %get-tuple-element.79.convolved_ref) | copy-start | bytes 3145732 | tf_op jit(solution)/shard_map/cond
  97.2 5.0 %collective-permute-start = (f32[96,256]{1,0:T(8,128)}, f32[96,256]{1,0:T(8,128)}, u32[]{:S(2)}, u32[]{:S(2)}) collective-permute-start(f32[96,256]{1,0:T(8,128)} %get-tuple-element.76.select_grad_ref.refs_1_), channel_id=1, source_target_pairs={{0,1},{1,0},{2,3},{3,2},{4,5},{5,4},{6,7},{7,6},{8,9},{9,8},{10,11... | collective-permute-start | bytes 294920 | tf_op jit(solution)/shard_map/cond/branch_1_fun/ppermute | solution.py:33
  99.6 10.2 %collective-permute-start.4 = (bf16[256,256]{1,0:T(8,128)(2,1)}, bf16[256,256]{1,0:T(8,128)(2,1)S(1)}, u32[]{:S(2)}, u32[]{:S(2)}) collective-permute-start(bf16[256,256]{1,0:T(8,128)(2,1)} %get-tuple-element.225), channel_id=1, source_target_pairs={{0,6},{2,4},{4,2},{6,0},{8,14},{10,12},{12,10},{14,8},{16,22},{18,... | collective-permute-start | bytes 393224 | tf_op jit(solution)/shard_map/cond/branch_1_fun/ppermute | solution.py:33
  99.6 10.2 %collective-permute-start.3 = (bf16[256,256]{1,0:T(8,128)(2,1)}, bf16[256,256]{1,0:T(8,128)(2,1)S(1)}, u32[]{:S(2)}, u32[]{:S(2)}) collective-permute-start(bf16[256,256]{1,0:T(8,128)(2,1)} %get-tuple-element.226), channel_id=1, source_target_pairs={{0,2},{2,0},{4,6},{6,4},{8,10},{10,8},{12,14},{14,12},{16,18},{18,... | collective-permute-start | bytes 393224 | tf_op jit(solution)/shard_map/cond/branch_1_fun/ppermute | solution.py:33
  100.3 9.5 %collective-permute-start.2 = (bf16[256,256]{1,0:T(8,128)(2,1)}, bf16[256,256]{1,0:T(8,128)(2,1)S(1)}, u32[]{:S(2)}, u32[]{:S(2)}) collective-permute-start(bf16[256,256]{1,0:T(8,128)(2,1)} %get-tuple-element.227), channel_id=1, source_target_pairs={{0,4},{2,6},{4,0},{6,2},{8,12},{10,14},{12,8},{14,10},{16,20},{18,... | collective-permute-start | bytes 393224 | tf_op jit(solution)/shard_map/cond/branch_1_fun/ppermute | solution.py:33
  102.2 5.7 %copy-start.27 = (f32[256,1]{1,0:T(8,128)S(1)}, f32[256,1]{1,0:T(8,128)}, u32[]{:S(2)}) copy-start(f32[256,1]{1,0:T(8,128)} %get-tuple-element.210) | copy-start | bytes 3076 | tf_op jit(solution)/shard_map/cond
  102.2 8.3 %copy-start.34 = (s32[256]{0:T(256)S(1)}, s32[256]{0:T(256)}, u32[]{:S(2)}) copy-start(s32[256]{0:T(256)} %get-tuple-element.61.ids_ref) | copy-start | bytes 3076 | tf_op jit(solution)/shard_map/cond
  106.3 12.3 %copy-start.31 = (f32[1024]{0:T(1024)S(1)}, f32[1024]{0:T(1024)}, u32[]{:S(2)}) copy-start(f32[1024]{0:T(1024)} %get-tuple-element.89) | copy-start | bytes 12292 | tf_op jit(solution)/shard_map/cond
  106.3 12.3 %copy-start.38 = (bf16[256,1024]{1,0:T(8,128)(2,1)S(1)}, bf16[256,1024]{1,0:T(8,128)(2,1)}, u32[]{:S(2)}) copy-start(bf16[256,1024]{1,0:T(8,128)(2,1)} %get-tuple-element.87) | copy-start | bytes 1572868 | tf_op jit(solution)/shard_map/cond
  106.3 12.3 %copy-start.39 = (bf16[256,1024]{1,0:T(8,128)(2,1)S(1)}, bf16[256,1024]{1,0:T(8,128)(2,1)}, u32[]{:S(2)}) copy-start(bf16[256,1024]{1,0:T(8,128)(2,1)} %get-tuple-element.85) | copy-start | bytes 1572868 | tf_op jit(solution)/shard_map/cond
  106.3 3.4 %collective-permute-start.1 = (f32[8,1024]{1,0:T(8,128)}, f32[8,1024]{1,0:T(8,128)S(1)}, u32[]{:S(2)}, u32[]{:S(2)}) collective-permute-start(f32[8,1024]{1,0:T(8,128)} %get-tuple-element.83), channel_id=1, source_target_pairs={{2,0},{4,2},{6,4},{8,6},{10,8},{12,10},{14,12},{16,14},{18,16},{20... | collective-permute-start | bytes 98312 | tf_op jit(solution)/shard_map/cond/branch_1_fun/ppermute | solution.py:28
  109.8 0.7 copy-start.23
  112.0 21.7 %collective-permute-start.5 = (bf16[256,1024]{1,0:T(8,128)(2,1)}, bf16[256,1024]{1,0:T(8,128)(2,1)S(1)}, u32[]{:S(2)}, u32[]{:S(2)}) collective-permute-start(bf16[256,1024]{1,0:T(8,128)(2,1)} %patched.1.wait_ref.own_ref), channel_id=1, source_target_pairs={{0,4},{2,6},{4,0},{6,2},{8,12},{10,14},{12,8},{14,10},{16,20},{18,... | collective-permute-start | bytes 1572872 | tf_op jit(solution)/shard_map/cond/branch_1_fun/ppermute | solution.py:33
  115.5 9.4 %collective-permute-start.8 = (bf16[128,1024]{1,0:T(8,128)(2,1)}, bf16[128,1024]{1,0:T(8,128)(2,1)S(1)}, u32[]{:S(2)}, u32[]{:S(2)}) collective-permute-start(bf16[128,1024]{1,0:T(8,128)(2,1)} %get-tuple-element.93), channel_id=1, source_target_pairs={{0,2},{2,0},{4,6},{6,4},{8,10},{10,8},{12,14},{14,12},{16,18},{18,... | collective-permute-start | bytes 786440 | tf_op jit(solution)/shard_map/cond/branch_1_fun/ppermute | solution.py:33
  122.9 16.8 %copy-start.11 = (f32[256,1024]{1,0:T(8,128)}, f32[256,1024]{1,0:T(8,128)S(1)}, u32[]{:S(2)}) copy-start(f32[256,1024]{1,0:T(8,128)S(1)} %get-tuple-element.235) | copy-start | bytes 3145732 | tf_op jit(solution)/shard_map/cond
  122.9 11.6 %copy-start.2 = (bf16[256,1024]{1,0:T(8,128)(2,1)S(1)}, bf16[256,1024]{1,0:T(8,128)(2,1)}, u32[]{:S(2)}) copy-start(bf16[256,1024]{1,0:T(8,128)(2,1)} %patched.1.wait_ref.own_ref) | copy-start | bytes 1572868 | tf_op jit(solution)/shard_map/cond
  122.9 4.9 %collective-permute-start.6 = (f32[1,1024]{1,0:T(1,128)S(1)}, f32[1,1024]{1,0:T(1,128)S(1)}, u32[]{:S(2)}, u32[]{:S(2)}) collective-permute-start(f32[1,1024]{1,0:T(1,128)S(1)} %bitcast.44), channel_id=1, source_target_pairs={{0,1},{1,0},{2,3},{3,2},{4,5},{5,4},{6,7},{7,6},{8,9},{9,8},{10,11... | collective-permute-start | bytes 12296 | tf_op jit(solution)/shard_map/cond/branch_1_fun/ppermute | solution.py:33
  124.4 4.0 %collective-permute-start.7 = (f32[1,256]{1,0:T(1,128)S(1)}, f32[1,256]{1,0:T(1,128)S(1)}, u32[]{:S(2)}, u32[]{:S(2)}) collective-permute-start(f32[1,256]{1,0:T(1,128)S(1)} %bitcast.46), channel_id=1, source_target_pairs={{0,1},{1,0},{2,3},{3,2},{4,5},{5,4},{6,7},{7,6},{8,9},{9,8},{10,11... | collective-permute-start | bytes 3080 | tf_op jit(solution)/shard_map/cond/branch_1_fun/ppermute | solution.py:33
  127.6 6.1 %collective-permute-start.9 = (bf16[64,1024]{1,0:T(8,128)(2,1)}, bf16[64,1024]{1,0:T(8,128)(2,1)S(1)}, u32[]{:S(2)}, u32[]{:S(2)}) collective-permute-start(bf16[64,1024]{1,0:T(8,128)(2,1)} %get-tuple-element.94), channel_id=1, source_target_pairs={{0,4},{2,6},{4,0},{6,2},{8,12},{10,14},{12,8},{14,10},{16,20},{18,... | collective-permute-start | bytes 393224 | tf_op jit(solution)/shard_map/cond/branch_1_fun/ppermute | solution.py:33
  128.4 5.3 %copy-start.36 = (f32[1,256]{1,0:T(1,128)}, f32[1,256]{1,0:T(1,128)S(1)}, u32[]{:S(2)}) copy-start(f32[1,256]{1,0:T(1,128)S(1)} %collective-permute-done.7.refs_2_) | copy-start | bytes 3076 | tf_op jit(solution)/shard_map/cond
  133.6 0.9 copy-start.3
  134.5 3.4 %copy-start.37 = (f32[1,256]{1,0:T(1,128)S(1)}, f32[1,256]{1,0:T(1,128)}, u32[]{:S(2)}) copy-start(f32[1,256]{1,0:T(1,128)} %copy-done.36) | copy-start | bytes 3076 | tf_op jit(solution)/shard_map/cond
  136.6 3.0 %collective-permute-start.10 = (bf16[512,1024]{1,0:T(8,128)(2,1)}, bf16[512,1024]{1,0:T(8,128)(2,1)}, u32[]{:S(2)}, u32[]{:S(2)}) collective-permute-start(bf16[512,1024]{1,0:T(8,128)(2,1)} %pad_maximum_fusion), channel_id=1, source_target_pairs={{0,2},{2,0},{4,6},{6,4},{8,10},{10,8},{12,14},{14,12},{16,18},{18,... | collective-permute-start | bytes 3145736 | tf_op jit(solution)/shard_map/cond/branch_1_fun/ppermute | solution.py:33
  137.9 5.3 %copy-start.13 = (bf16[256,1024]{1,0:T(8,128)(2,1)S(1)}, bf16[256,1024]{1,0:T(8,128)(2,1)}, u32[]{:S(2)}) copy-start(bf16[256,1024]{1,0:T(8,128)(2,1)} %get-tuple-element.102.refs_0_) | copy-start | bytes 1572868 | tf_op jit(solution)/shard_map/cond
  139.6 11.0 %copy-start.1 = (bf16[1024,1024]{1,0:T(8,128)(2,1)S(1)}, bf16[1024,1024]{1,0:T(8,128)(2,1)}, u32[]{:S(2)}) copy-start(bf16[1024,1024]{1,0:T(8,128)(2,1)} %get-tuple-element.103) | copy-start | bytes 6291460 | tf_op jit(solution)/shard_map/cond
  143.3 5.8 %copy-start.40 = (bf16[80,1024]{1,0:T(8,128)(2,1)S(1)}, bf16[80,1024]{1,0:T(8,128)(2,1)}, u32[]{:S(2)}) copy-start(bf16[80,1024]{1,0:T(8,128)(2,1)} %get-tuple-element.99) | copy-start | bytes 491524 | tf_op jit(solution)/shard_map/cond
  143.3 14.6 %collective-permute-start.11 = (bf16[80,1024]{1,0:T(8,128)(2,1)}, bf16[80,1024]{1,0:T(8,128)(2,1)S(1)}, u32[]{:S(2)}, u32[]{:S(2)}) collective-permute-start(bf16[80,1024]{1,0:T(8,128)(2,1)} %get-tuple-element.97), channel_id=1, source_target_pairs={{0,8},{2,10},{4,12},{6,14},{8,0},{10,2},{12,4},{14,6},{16,24},{18,... | collective-permute-start | bytes 491528 | tf_op jit(solution)/shard_map/cond/branch_1_fun/ppermute | solution.py:33
  146.2 17.1 %collective-permute-start.12 = (bf16[80,1024]{1,0:T(8,128)(2,1)}, bf16[80,1024]{1,0:T(8,128)(2,1)S(1)}, u32[]{:S(2)}, u32[]{:S(2)}) collective-permute-start(bf16[80,1024]{1,0:T(8,128)(2,1)} %get-tuple-element.98), channel_id=1, source_target_pairs={{0,16},{2,18},{4,20},{6,22},{8,24},{10,26},{12,28},{14,30},{16,0},... | collective-permute-start | bytes 491528 | tf_op jit(solution)/shard_map/cond/branch_1_fun/ppermute | solution.py:33
  149.0 14.2 %collective-permute-start.13 = (bf16[80,1024]{1,0:T(8,128)(2,1)S(1)}, bf16[80,1024]{1,0:T(8,128)(2,1)S(1)}, u32[]{:S(2)}, u32[]{:S(2)}) collective-permute-start(bf16[80,1024]{1,0:T(8,128)(2,1)S(1)} %copy-done.40), channel_id=1, source_target_pairs={{0,24},{2,26},{4,28},{6,30},{8,16},{10,18},{12,20},{14,22},{16,8},... | collective-permute-start | bytes 491528 | tf_op jit(solution)/shard_map/cond/branch_1_fun/ppermute | solution.py:33
  149.3 20.2 %collective-permute-start.18 = (bf16[256,512]{1,0:T(8,128)(2,1)}, bf16[256,512]{1,0:T(8,128)(2,1)S(1)}, u32[]{:S(2)}, u32[]{:S(2)}) collective-permute-start(bf16[256,512]{1,0:T(8,128)(2,1)} %after.8), channel_id=1, source_target_pairs={{0,1},{1,0},{2,3},{3,2},{4,5},{5,4},{6,7},{7,6},{8,9},{9,8},{10,11... | collective-permute-start | bytes 786440 | tf_op jit(solution)/shard_map/cond/branch_1_fun/ppermute | solution.py:33
  150.6 12.7 %copy-start.4 = (f32[80,1024]{1,0:T(8,128)S(1)}, f32[80,1024]{1,0:T(8,128)}, u32[]{:S(2)}) copy-start(f32[80,1024]{1,0:T(8,128)} %get-tuple-element.96.refs_1_) | copy-start | bytes 983044 | tf_op jit(solution)/shard_map/cond
  150.6 18.9 %copy-start.8 = (bf16[256,512]{1,0:T(8,128)(2,1)S(1)}, bf16[256,512]{1,0:T(8,128)(2,1)}, u32[]{:S(2)}) copy-start(bf16[256,512]{1,0:T(8,128)(2,1)} %get-tuple-element.100) | copy-start | bytes 786436 | tf_op jit(solution)/shard_map/cond
  150.6 18.9 %copy-start.12 = (f32[256,1024]{1,0:T(8,128)S(1)}, f32[256,1024]{1,0:T(8,128)}, u32[]{:S(2)}) copy-start(f32[256,1024]{1,0:T(8,128)} %copy-done.11) | copy-start | bytes 3145732 | tf_op jit(solution)/shard_map/cond
  150.6 18.9 %copy-start.16 = (bf16[256,512]{1,0:T(8,128)(2,1)S(1)}, bf16[256,512]{1,0:T(8,128)(2,1)}, u32[]{:S(2)}) copy-start(bf16[256,512]{1,0:T(8,128)(2,1)} %get-tuple-element.104) | copy-start | bytes 786436 | tf_op jit(solution)/shard_map/cond
  150.6 18.9 %copy-start.35 = (f32[256,1]{0,1:T(1,128)S(1)}, f32[256,1]{0,1:T(1,128)}, u32[]{:S(2)}) copy-start(f32[256,1]{0,1:T(1,128)} %multiply_multiply_fusion) | copy-start | bytes 3076 | tf_op jit(solution)/shard_map/cond
  151.4 18.1 %collective-permute-start.17 = (bf16[256,512]{1,0:T(8,128)(2,1)S(1)}, bf16[256,512]{1,0:T(8,128)(2,1)S(1)}, u32[]{:S(2)}, u32[]{:S(2)}) collective-permute-start(bf16[256,512]{1,0:T(8,128)(2,1)S(1)} %select_convert_fusion.1), channel_id=1, source_target_pairs={{0,1},{1,0},{2,3},{3,2},{4,5},{5,4},{6,7},{7,6},{8,9},{9,8},{10,11... | collective-permute-start | bytes 786440 | tf_op jit(solution)/shard_map/cond/branch_1_fun/ppermute | solution.py:33
  163.4 12.1 %collective-permute-start.16 = (bf16[80,1024]{1,0:T(8,128)(2,1)S(1)}, bf16[80,1024]{1,0:T(8,128)(2,1)S(1)}, u32[]{:S(2)}, u32[]{:S(2)}) collective-permute-start(bf16[80,1024]{1,0:T(8,128)(2,1)S(1)} %pad_maximum_fusion.4), channel_id=1, source_target_pairs={{0,8},{2,10},{4,12},{6,14},{8,0},{10,2},{12,4},{14,6},{16,24},{18,... | collective-permute-start | bytes 491528 | tf_op jit(solution)/shard_map/cond/branch_1_fun/ppermute | solution.py:33
  167.1 16.9 %collective-permute-start.15 = (bf16[80,1024]{1,0:T(8,128)(2,1)S(1)}, bf16[80,1024]{1,0:T(8,128)(2,1)S(1)}, u32[]{:S(2)}, u32[]{:S(2)}) collective-permute-start(bf16[80,1024]{1,0:T(8,128)(2,1)S(1)} %pad_maximum_fusion.4), channel_id=1, source_target_pairs={{0,16},{2,18},{4,20},{6,22},{8,24},{10,26},{12,28},{14,30},{16,0},... | collective-permute-start | bytes 491528 | tf_op jit(solution)/shard_map/cond/branch_1_fun/ppermute | solution.py:33
  167.7 20.7 %collective-permute-start.14 = (bf16[80,1024]{1,0:T(8,128)(2,1)S(1)}, bf16[80,1024]{1,0:T(8,128)(2,1)S(1)}, u32[]{:S(2)}, u32[]{:S(2)}) collective-permute-start(bf16[80,1024]{1,0:T(8,128)(2,1)S(1)} %pad_maximum_fusion.4), channel_id=1, source_target_pairs={{0,24},{2,26},{4,28},{6,30},{8,16},{10,18},{12,20},{14,22},{16,8},... | collective-permute-start | bytes 491528 | tf_op jit(solution)/shard_map/cond/branch_1_fun/ppermute | solution.py:33
  188.6 17.1 %collective-permute-start.28 = (bf16[320,1024]{1,0:T(8,128)(2,1)S(1)}, bf16[320,1024]{1,0:T(8,128)(2,1)S(1)}, u32[]{:S(2)}, u32[]{:S(2)}) collective-permute-start(bf16[320,1024]{1,0:T(8,128)(2,1)S(1)} %get-tuple-element.174.first_ref.rest_0_), channel_id=1, source_target_pairs={{0,4},{2,6},{4,0},{6,2},{8,12},{10,14},{12,8},{14,10},{16,20},{18,... | collective-permute-start | bytes 1966088 | tf_op jit(solution)/shard_map/ppermute | solution.py:33
  189.5 16.2 %collective-permute-start.30 = (bf16[320,1024]{1,0:T(8,128)(2,1)S(1)}, bf16[320,1024]{1,0:T(8,128)(2,1)S(1)}, u32[]{:S(2)}, u32[]{:S(2)}) collective-permute-start(bf16[320,1024]{1,0:T(8,128)(2,1)S(1)} %get-tuple-element.174.first_ref.rest_0_), channel_id=1, source_target_pairs={{0,2},{2,0},{4,6},{6,4},{8,10},{10,8},{12,14},{14,12},{16,18},{18,... | collective-permute-start | bytes 1966088 | tf_op jit(solution)/shard_map/ppermute | solution.py:33
  205.7 10.5 %copy-start.5 = (bf16[320,1024]{1,0:T(8,128)(2,1)}, bf16[320,1024]{1,0:T(8,128)(2,1)S(1)}, u32[]{:S(2)}) copy-start(bf16[320,1024]{1,0:T(8,128)(2,1)S(1)} %collective-permute-done.28.first_ref.rest_2_) | copy-start | bytes 1966084
  205.7 10.5 %collective-permute-start.29 = (bf16[320,1024]{1,0:T(8,128)(2,1)S(1)}, bf16[320,1024]{1,0:T(8,128)(2,1)S(1)}, u32[]{:S(2)}, u32[]{:S(2)}) collective-permute-start(bf16[320,1024]{1,0:T(8,128)(2,1)S(1)} %collective-permute-done.28.first_ref.rest_2_), channel_id=1, source_target_pairs={{0,2},{2,0},{4,6},{6,4},{8,10},{10,8},{12,14},{14,12},{16,18},{18,... | collective-permute-start | bytes 1966088 | tf_op jit(solution)/shard_map/ppermute | solution.py:33
  205.7 5.1 %copy-start.7 = (bf16[320,1024]{1,0:T(8,128)(2,1)}, bf16[320,1024]{1,0:T(8,128)(2,1)S(1)}, u32[]{:S(2)}) copy-start(bf16[320,1024]{1,0:T(8,128)(2,1)S(1)} %collective-permute-done.30.second_ref.rest_1_) | copy-start | bytes 1966084
  216.2 0.8 copy-start.6
  (9 other events, 5.9 us)
Sparse Core Ops, SparseCore 0:
  73.8 136.9 all-reduce.2
